TPU v7x, 32 devices: a whole 2x2x4 slice. The times are simulated.
32 devices in a mesh: leaf: 8 (over y, x, core), grp: 4 (over z).
Axes of the slice: x: 2, y: 2, z: 4, core: 2. Of those that a mesh axis runs over, the one named last changes fastest.
Arguments:
- rhs_local: float32 [8, 4, 1024, 128], P('leaf', None, 'grp'), may hold values from -6 to 6
- diag_inv_local: float32 [8, 4, 1024, 1024], P('leaf', None, 'grp'), may hold values from -0.1875 to 0.1875
- sub_local: float32 [8, 3, 1024, 1024], P('leaf', None, 'grp'), may hold values from -0.1875 to 0.1875
- tiles: float32 [8, 4, 3, 128, 1024], P('leaf', 'grp'), may hold values from -0.046875 to 0.046875
- tile_block: int32 [8, 4, 3], P('leaf', 'grp'), may hold values from 0 to 15
- tile_source: int32 [8, 4, 3], P('leaf', 'grp'), may hold values from 0 to 3
- tile_count: int32 [8, 4], P('leaf', 'grp'), may hold values from 1 to 3, as said below
- rhs_anc: float32 [2, 1024, 128], P(None, 'grp', 'leaf'), may hold values from -6 to 6
- diag_inv_anc: float32 [2, 1024, 1024], P(None, 'grp'), may hold values from -0.1875 to 0.1875
- sub_anc: float32 [1, 1024, 1024], P(None, 'grp'), may hold values from -0.1875 to 0.1875
Outputs:
- solution_local: float32 [8, 4, 1024, 128], P('leaf', None, 'grp')
- solution_anc: float32 [2, 1024, 128], P(None, 'grp', 'leaf')
Inputs may be any that keep to these rules, and one draw needn't show every extreme that they name: `tile_count`: some device holds exactly 3 live tiles.
All inputs are finite; a program needn't handle non-finite values.
Results may differ from a plain program's by a relative error of at most 0.0003.
Values sent between devices are 32-bit elements; how exact they have to be, the bound alone decides.
No kernel may reach another device: no remote copies, remote signals or barrier semaphores. Data moves between devices by JAX's collectives and lax.ppermute only.
A program may use at most 64 MiB of HBM per device.

v0:
```python
import jax
import jax.numpy as jnp
from jax import lax
from jax.sharding import PartitionSpec as P

highest = lax.Precision.HIGHEST


def product(left, right):
    return jnp.dot(left, right, precision=highest, preferred_element_type=jnp.float32)


def fold_columns(matrix, portion):
    return product(matrix, portion)


def on_device(
    rhs_local,
    diag_inv_local,
    sub_local,
    tiles,
    tile_block,
    tile_source,
    tile_count,
    rhs_anc,
    diag_inv_anc,
    sub_anc,
):
    rhs_group = rhs_local[0]
    inverse_group = diag_inv_local[0]
    below_group = sub_local[0]
    supernodes = rhs_group.shape[0]
    block_order = inverse_group.shape[-1]
    rhs_count = rhs_group.shape[-1]
    solved = []
    gathered = []
    update = jnp.zeros_like(rhs_group[0])
    for current in range(supernodes):
        residual = rhs_group[current] - update
        owned = fold_columns(
            inverse_group[current], lax.all_gather(residual, "grp", axis=0, tiled=True)
        )
        solved.append(owned)
        full_solution = lax.all_gather(owned, "grp", axis=0, tiled=True)
        gathered.append(full_solution)
        if current + 1 < supernodes:
            update = product(below_group[current], full_solution)
    stacked = jnp.stack(gathered)
    tiles_mine = tiles[0, 0]
    blocks = tile_block[0, 0]
    sources = tile_source[0, 0]
    live_count = tile_count[0, 0]
    slots = tiles_mine.shape[0]
    tile_rows = tiles_mine.shape[1]
    ancestors = rhs_anc.shape[0]
    members = lax.axis_size("grp")
    owned_rows = block_order // members
    active = jnp.arange(slots, dtype=jnp.int32) < live_count
    chosen = stacked[sources]
    tile_terms = jnp.einsum(
        "mtk,mkr->mtr", tiles_mine, chosen, precision=highest, preferred_element_type=jnp.float32
    )
    piece = min(tile_rows, owned_rows)
    per_super = block_order // tile_rows
    ancestor_id = blocks // per_super
    start = blocks % per_super * tile_rows
    low = jnp.arange(members, dtype=jnp.int32)[:, None] * owned_rows
    valid = (
        (start[None, :] < low + owned_rows) & (start[None, :] + tile_rows > low) & active[None, :]
    )
    offset = jnp.clip(low - start[None, :], 0, tile_rows - piece)

    def cut_rows(term, begin):
        return lax.dynamic_slice_in_dim(term, begin, piece, 0)

    pieces = jax.vmap(jax.vmap(cut_rows, (0, 0)), (None, 0))(tile_terms, offset)
    pieces = pieces * valid.astype(jnp.float32)[:, :, None, None]
    position = jnp.maximum(start[None, :] - low, 0)
    place = ancestor_id[None, :] * (owned_rows // piece) + position // piece
    codes = jnp.where(valid, place, -1).astype(jnp.float32)
    received, got_codes = (
        lax.all_to_all(pieces, "grp", split_axis=0, concat_axis=0, tiled=True),
        lax.all_to_all(codes, "grp", split_axis=0, concat_axis=0, tiled=True),
    )
    flat = received.reshape(-1, piece, rhs_count)
    places_total = ancestors * owned_rows // piece
    onehot = (
        got_codes.reshape(-1)[:, None] == jnp.arange(places_total, dtype=jnp.float32)[None, :]
    ).astype(jnp.float32)
    summed = jnp.einsum(
        "nq,npr->qpr", onehot, flat, precision=highest, preferred_element_type=jnp.float32
    )
    summed = summed.reshape(ancestors, owned_rows, rhs_count)
    part_mine = lax.psum_scatter(summed, "leaf", scatter_dimension=2, tiled=True)
    ancestors_solved = []
    update = jnp.zeros_like(rhs_anc[0])
    for ancestor in range(ancestors):
        residual = rhs_anc[ancestor] - part_mine[ancestor] - update
        solution = fold_columns(
            diag_inv_anc[ancestor], lax.all_gather(residual, "grp", axis=0, tiled=True)
        )
        ancestors_solved.append(solution)
        if ancestor + 1 < ancestors:
            update = fold_columns(
                sub_anc[ancestor], lax.all_gather(solution, "grp", axis=0, tiled=True)
            )
    return (jnp.stack(solved)[None], jnp.stack(ancestors_solved))


def solution(mesh):
    return jax.shard_map(
        on_device,
        mesh=mesh,
        in_specs=(
            P("leaf", None, "grp", None),
            P("leaf", None, "grp", None),
            P("leaf", None, "grp", None),
            P("leaf", "grp", None, None, None),
            P("leaf", "grp", None),
            P("leaf", "grp", None),
            P("leaf", "grp"),
            P(None, "grp", "leaf"),
            P(None, "grp", None),
            P(None, "grp", None),
        ),
        out_specs=(P("leaf", None, "grp", None), P(None, "grp", "leaf")),
        check_vma=False,
    )
```

profile of v0, /device:TPU:0, one launch (start us, length us, event | category | flops | bytes accessed | tf_op | source)
XLA Modules:
  0.0 297.8 jit_solution(1554689734355857972)
XLA Ops:
  7.2 0.0 copy-start
  7.2 0.8 broadcast_add_fusion.1
  8.6 0.7 fusion.39
  9.3 6.3 %all-to-all-start = ((f32[4,1,3]{2,1,0:T(1,128)}), f32[4,1,3]{2,1,0:T(1,128)S(1)}, u32[]{:S(2)}, u32[]{:S(2)}) async-start(f32[4,1,3]{2,1,0:T(1,128)} %fusion.39), calls=%async_computation | async-start | bytes 4096 | tf_op jit(solution)/shard_map/all_to_all | solution.py:83
  15.6 0.1 shift-left_or_fusion
  15.7 0.1 and_convert_fusion
  15.8 1.8 fusion.47
  17.6 15.7 %all-gather = f32[1,1,1024,128]{3,2,1,0:T(8,128)S(1)} all-gather(f32[1,1,256,128]{3,2,1,0:T(8,128)S(1)} %get-tuple-element.7), channel_id=2, replica_groups=mesh['leaf'=8,'grp'=4] {'grp'}, dimensions={2}, use_global_device_ids=true | all-gather | bytes 655360 | tf_op jit(solution)/shard_map/all_gather | solution.py:41
  33.2 2.2 fusion.22
  35.4 16.1 %all_gather.34 = f32[1024,128]{1,0:T(8,128)S(1)} all-gather(f32[256,128]{1,0:T(8,128)S(1)} %fusion.22), channel_id=1, replica_groups=mesh['leaf'=8,'grp'=4] {'grp'}, dimensions={0}, use_global_device_ids=true | all-gather | bytes 655360 | tf_op jit(solution)/shard_map/all_gather | solution.py:44
  51.6 0.1 copy.45
  51.7 2.2 fusion.7
  53.9 16.2 %all_gather.35 = f32[1024,128]{0,1:T(8,128)S(1)} all-gather(f32[256,128]{0,1:T(8,128)S(1)} %fusion.7), channel_id=1, replica_groups=mesh['leaf'=8,'grp'=4] {'grp'}, dimensions={0}, use_global_device_ids=true | all-gather | bytes 655360 | tf_op jit(solution)/shard_map/all_gather | solution.py:41
  70.1 2.2 fusion.19
  72.3 16.5 %all_gather.36 = f32[1024,128]{1,0:T(8,128)S(1)} all-gather(f32[256,128]{1,0:T(8,128)S(1)} %bitcast.141), channel_id=1, replica_groups=mesh['leaf'=8,'grp'=4] {'grp'}, dimensions={0}, use_global_device_ids=true | all-gather | bytes 655360 | tf_op jit(solution)/shard_map/all_gather | solution.py:44
  88.8 0.1 copy.46
  88.9 2.2 fusion.6
  91.2 16.5 %all_gather.37 = f32[1024,128]{0,1:T(8,128)S(1)} all-gather(f32[256,128]{0,1:T(8,128)S(1)} %fusion.6), channel_id=1, replica_groups=mesh['leaf'=8,'grp'=4] {'grp'}, dimensions={0}, use_global_device_ids=true | all-gather | bytes 655360 | tf_op jit(solution)/shard_map/all_gather | solution.py:41
  107.7 2.2 fusion.16
  109.9 16.2 %all_gather.38 = f32[1024,128]{1,0:T(8,128)S(1)} all-gather(f32[256,128]{1,0:T(8,128)S(1)} %bitcast.143), channel_id=1, replica_groups=mesh['leaf'=8,'grp'=4] {'grp'}, dimensions={0}, use_global_device_ids=true | all-gather | bytes 655360 | tf_op jit(solution)/shard_map/all_gather | solution.py:44
  126.2 1.7 copy.47
  127.8 2.2 fusion.5
  130.1 15.9 %all_gather.39 = f32[1024,128]{0,1:T(8,128)S(1)} all-gather(f32[256,128]{0,1:T(8,128)S(1)} %fusion.5), channel_id=1, replica_groups=mesh['leaf'=8,'grp'=4] {'grp'}, dimensions={0}, use_global_device_ids=true | all-gather | bytes 655360 | tf_op jit(solution)/shard_map/all_gather | solution.py:41
  146.0 2.2 fusion.13
  148.2 0.0 copy-start.2
  148.2 0.6 copy-done.2
  148.9 16.3 %all_gather.40 = f32[1024,128]{1,0:T(8,128)S(1)} all-gather(f32[256,128]{1,0:T(8,128)S(1)} %bitcast.145), channel_id=1, replica_groups=mesh['leaf'=8,'grp'=4] {'grp'}, dimensions={0}, use_global_device_ids=true | all-gather | bytes 655360 | tf_op jit(solution)/shard_map/all_gather | solution.py:44
  165.2 0.0 copy-done.6
  165.2 1.5 pad_maximum_fusion
  166.7 2.2 gather_fusion
  168.9 0.0 copy-done
  168.9 3.3 %fusion.2 = f32[3,128,128]{1,2,0:T(8,128)} fusion(f32[3,1024,128]{2,1,0:T(8,128)S(1)} %gather_fusion, f32[1,1,3,128,1024]{4,3,2,1,0:T(8,128)S(1)} %copy-done), kind=kOutput, calls=%fused_computation.5 | convolution fusion | flops 603979776 | bytes 3342336 | tf_op jit(solution)/shard_map/mtk,mkr->mtr/dot_general | solution.py:60
  172.2 1.1 copy.34
  173.3 0.1 reshape.462
  173.4 0.6 gather_fusion.1
  174.0 1.0 broadcast_multiply_fusion
  175.0 0.0 all-to-all-done
  175.0 4.9 %all-to-all-start.1 = ((f32[4,3,128,128]{3,2,1,0:T(8,128)}), f32[4,3,128,128]{3,2,1,0:T(8,128)S(1)}, u32[]{:S(2)}, u32[]{:S(2)}) async-start(f32[4,3,128,128]{3,2,1,0:T(8,128)} %broadcast_multiply_fusion), calls=%async_computation.1 | async-start | bytes 1572864 | tf_op jit(solution)/shard_map/all_to_all | solution.py:82
  179.9 0.0 all-reduce.4.cloned.1.call-start
  180.0 0.5 broadcast.493
  180.5 0.7 reduce.3
  181.1 0.1 eq.17
  181.2 11.8 %all-to-all-done.1 = f32[4,3,128,128]{3,2,1,0:T(8,128)S(1)} async-done(((f32[4,3,128,128]{3,2,1,0:T(8,128)}), f32[4,3,128,128]{3,2,1,0:T(8,128)S(1)}, u32[]{:S(2)}, u32[]{:S(2)}) %all-to-all-start.1) | async-done | bytes 786464 | tf_op jit(solution)/shard_map/all_to_all | solution.py:82
  193.0 0.9 fusion.24
  194.0 0.0 copy-start.4
  194.0 0.0 copy-start.5
  194.0 0.8 copy.37
  194.8 0.0 all-reduce.4.cloned.1.call-update
  194.9 0.0 copy-done.7
  194.9 0.6 dynamic-slice
  196.1 0.0 copy-done.3
  196.1 0.8 maximum_bitcast_fusion
  197.0 50.7 %all-reduce.4.cloned.1.call-done = f32[2,256,128]{1,0,2:T(2,128)} async-done(((f32[2,256,128]{1,0,2:T(2,128)}), f32[2,256,128]{1,0,2:T(2,128)}) %all-reduce.4.cloned.1.call-update) | async-done | bytes 262160
  247.7 0.0 slice-done
  247.7 1.0 constant_dynamic-slice_fusion
  248.7 11.4 %all-gather.1 = f32[1,1024,16]{1,0,2:T(1,128)S(1)} all-gather(f32[1,256,16]{1,0,2:T(1,128)S(1)} %get-tuple-element.9), channel_id=3, replica_groups=mesh['leaf'=8,'grp'=4] {'grp'}, dimensions={1}, use_global_device_ids=true | all-gather | bytes 81920 | tf_op jit(solution)/shard_map/all_gather | solution.py:100
  260.0 2.1 fusion.11
  262.2 13.1 %all_gather.42 = f32[1024,16]{0,1:T(8,128)S(1)} all-gather(f32[256,16]{0,1:T(8,128)S(1)} %bitcast.148), channel_id=1, replica_groups=mesh['leaf'=8,'grp'=4] {'grp'}, dimensions={0}, use_global_device_ids=true | all-gather | bytes 81920 | tf_op jit(solution)/shard_map/all_gather | solution.py:105
  275.3 0.0 copy-done.4
  275.3 0.0 copy-done.5
  275.3 0.9 fusion.8
  276.2 13.1 %all_gather.43 = f32[1024,16]{0,1:T(8,128)S(1)} all-gather(f32[256,16]{0,1:T(8,128)S(1)} %fusion.8), channel_id=1, replica_groups=mesh['leaf'=8,'grp'=4] {'grp'}, dimensions={0}, use_global_device_ids=true | all-gather | bytes 81920 | tf_op jit(solution)/shard_map/all_gather | solution.py:100
  289.4 0.9 convolution_bitcast_fusion.3
  290.3 0.6 pad_maximum_fusion.1
  (11 shorter events, 0.1 us)
Async XLA Ops:
  7.2 161.8 %copy-start = (f32[1,1,3,128,1024]{4,3,2,1,0:T(8,128)S(1)}, f32[1,1,3,128,1024]{4,3,2,1,0:T(8,128)}, u32[]{:S(2)}) copy-start(f32[1,1,3,128,1024]{4,3,2,1,0:T(8,128)} %param.13) | copy-start | bytes 4718596
  9.3 165.7 %all-to-all-start = ((f32[4,1,3]{2,1,0:T(1,128)}), f32[4,1,3]{2,1,0:T(1,128)S(1)}, u32[]{:S(2)}, u32[]{:S(2)}) async-start(f32[4,1,3]{2,1,0:T(1,128)} %fusion.39), calls=%async_computation | async-start | bytes 4096 | tf_op jit(solution)/shard_map/all_to_all | solution.py:83
  127.8 37.4 %copy-start.6 = (s32[1,1,3]{2,1,0:T(1,128)S(1)}, s32[1,1,3]{2,1,0:T(1,128)}, u32[]{:S(2)}) copy-start(s32[1,1,3]{2,1,0:T(1,128)} %param.15) | copy-start | bytes 40
  148.2 0.6 copy-start.2
  175.0 19.9 %copy-start.7 = (u32[32]{0:T(128)S(1)}, u32[32]{0:T(128)}, u32[]{:S(2)}) copy-start(u32[32]{0:T(128)} %constant.90) | copy-start | bytes 388
  175.0 21.1 %copy-start.3 = (f32[128,256]{0,1:T(8,128)S(1)}, f32[128,256]{0,1:T(8,128)}, u32[]{:S(2)}) copy-start(f32[128,256]{0,1:T(8,128)} %copy-done.2) | copy-start | bytes 393220
  175.0 18.0 %all-to-all-start.1 = ((f32[4,3,128,128]{3,2,1,0:T(8,128)}), f32[4,3,128,128]{3,2,1,0:T(8,128)S(1)}, u32[]{:S(2)}, u32[]{:S(2)}) async-start(f32[4,3,128,128]{3,2,1,0:T(8,128)} %broadcast_multiply_fusion), calls=%async_computation.1 | async-start | bytes 1572864 | tf_op jit(solution)/shard_map/all_to_all | solution.py:82
  179.9 67.7 %slice-start = ((f32[2,256,16]{1,2,0:T(8,128)}), f32[1,256,16]{1,2,0:T(8,128)S(1)}, s32[]{:S(2)}) async-start(f32[2,256,16]{1,2,0:T(8,128)} %param.17), calls=%async_computation.3 | async-start | bytes 32768 | tf_op jit(solution)/shard_map/slice | solution.py:98
  179.9 67.7 %all-reduce.4.cloned.1.call-start = ((), (), s32[]{:S(2)}) async-start(), calls=%async_computation.2 | async-start | bytes 524288
  194.0 81.4 %copy-start.4 = (f32[1,256,1024]{2,1,0:T(8,128)S(1)}, f32[1,256,1024]{2,1,0:T(8,128)}, u32[]{:S(2)}) copy-start(f32[1,256,1024]{2,1,0:T(8,128)} %param.19) | copy-start | bytes 3145732
  194.0 81.4 %copy-start.5 = (f32[2,256,16]{1,2,0:T(8,128)S(1)}, f32[2,256,16]{1,2,0:T(8,128)}, u32[]{:S(2)}) copy-start(f32[2,256,16]{1,2,0:T(8,128)} %param.17) | copy-start | bytes 98308
  247.7 41.7 %copy-start.1 = (f32[2,256,1024]{2,1,0:T(8,128)S(1)}, f32[2,256,1024]{2,1,0:T(8,128)}, u32[]{:S(2)}) copy-start(f32[2,256,1024]{2,1,0:T(8,128)} %param.18) | copy-start | bytes 6291460
Sparse Core Ops, SparseCore 0:
  195.0 52.6 all-reduce.3
where the time goes:
time: 299 us; the launch traced here: 298 us
  blocking collectives  167 us (56%)
  waiting for transfers between devices  62.6 us (21%)
  matrix products  23.7 us (8%)
  between operations  15.5 us (5%)
  starting transfers between devices  11.2 us (4%)
  local copies, waits for them, and re-layouts  10.3 us (3%)
  other arithmetic  7.21 us (2%)
    all_gather x6, blocking collectives, on_device(): lax.all_gather(residual, 'grp', axis=0, tiled=True)  88.8 us
    all_gather x4, blocking collectives, on_device(): full_solution = lax.all_gather(owned, 'grp', axis=0, tiled=True)  65.2 us
    unnamed x2, waiting for transfers between devices  50.7 us
    dot_general x10, matrix products, product(): jnp.dot(left, right, precision=highest, preferred_element_type=jnp.float32)  19.5 us
    all_gather x1, blocking collectives, on_device(): lax.all_gather(solution, 'grp', axis=0, tiled=True)  13.1 us
    all_to_all x1, waiting for transfers between devices, on_device(): lax.all_to_all(pieces, 'grp', split_axis=0, concat_axis=0, tiled=True)  11.8 us
    all_to_all x1, starting transfers between devices, on_device(): lax.all_to_all(codes, 'grp', split_axis=0, concat_axis=0, tiled=True)  6.32 us
  transfers between devices with their start and end apart: 3, of which 2 were waited for; matrix products, arithmetic and copies ran while one was open for 11% of the time, Pallas kernels for 0%

commit v1 on v0

v1 whole, which is shorter than its diff:
```python
import jax
import jax.numpy as jnp
from jax import lax
from jax.sharding import PartitionSpec as P

high = lax.Precision.HIGH


def product(left, right):
    return jnp.dot(left, right, precision=high, preferred_element_type=jnp.float32)


def contract_last(left, right):
    return lax.dot_general(
        left,
        right,
        (((left.ndim - 1,), (right.ndim - 1,)), ((), ())),
        precision=high,
        preferred_element_type=jnp.float32,
    )


def send(value, axis, shift):
    count = lax.axis_size(axis)
    return lax.ppermute(value, axis, [(i, (i + shift) % count) for i in range(count)])


def gather_pieces(value):
    members = lax.axis_size("grp")
    return [value] + [send(value, "grp", shift) for shift in range(1, members)]


def column_block(matrix, shift, width):
    members = lax.axis_size("grp")
    owner = lax.rem(lax.axis_index("grp") - shift + members, members)
    return lax.dynamic_slice_in_dim(matrix, owner * width, width, 1)


def apply_rows(matrix, pieces):
    total = None
    for shift, piece in enumerate(pieces):
        term = product(column_block(matrix, shift, piece.shape[0]), piece)
        total = term if total is None else total + term
    return total


def in_order(pieces):
    members = lax.axis_size("grp")
    me = lax.axis_index("grp")
    stacked = jnp.stack(pieces)
    owners = lax.rem(me - jnp.arange(members, dtype=jnp.int32) + members, members)
    return stacked[owners].reshape(-1, pieces[0].shape[-1])


def on_device(
    rhs_local,
    diag_inv_local,
    sub_local,
    tiles,
    tile_block,
    tile_source,
    tile_count,
    rhs_anc,
    diag_inv_anc,
    sub_anc,
):
    rhs_group = rhs_local[0]
    inverse_group = diag_inv_local[0]
    below_group = sub_local[0]
    supernodes = rhs_group.shape[0]
    order = inverse_group.shape[-1]
    rhs_count = rhs_group.shape[-1]
    members = lax.axis_size("grp")
    groups = lax.axis_size("leaf")
    me = lax.axis_index("grp")
    leaf = lax.axis_index("leaf")
    rows = order // members

    wide = order // groups
    sub_columns = lax.dynamic_slice_in_dim(sub_anc[0], leaf * wide, wide, 1)
    inverse_columns = lax.dynamic_slice_in_dim(diag_inv_anc[0], leaf * wide, wide, 1)
    half = apply_rows(diag_inv_anc[1], gather_pieces(sub_columns))
    half = lax.all_gather(half, "leaf", axis=1, tiled=True)
    coupled = apply_rows(half, gather_pieces(inverse_columns))
    coupled = lax.all_gather(coupled, "leaf", axis=1, tiled=True)

    tiles_mine = tiles[0, 0]
    slots, tile_rows = tiles_mine.shape[:2]
    blocks_mine = jnp.where(
        jnp.arange(slots, dtype=jnp.int32) < tile_count[0, 0], tile_block[0, 0], -1
    )
    blocks_all = lax.all_gather(blocks_mine.astype(jnp.float32), "leaf", axis=0, tiled=True)

    solved = []
    gathered = []
    residual = rhs_group[0]
    for current in range(supernodes):
        owned = apply_rows(inverse_group[current], gather_pieces(residual))
        solved.append(owned)
        pieces = gather_pieces(owned)
        gathered.append(in_order(pieces))
        if current + 1 < supernodes:
            residual = rhs_group[current + 1] - apply_rows(below_group[current], pieces)

    chosen = jnp.stack(gathered)[tile_source[0, 0]]
    terms = jnp.einsum(
        "mtk,mkr->rmt", tiles_mine, chosen, precision=high, preferred_element_type=jnp.float32
    )
    received = lax.all_to_all(terms, "leaf", split_axis=0, concat_axis=0, tiled=True)
    part = rhs_count // groups
    received = received.reshape(groups, part, slots, tile_rows)
    ancestors = rhs_anc.shape[0]
    block_count = ancestors * order // tile_rows
    onehot = (
        blocks_all[:, None] == jnp.arange(block_count, dtype=jnp.float32)[None, :]
    ).astype(jnp.float32)
    summed = jnp.einsum(
        "gmq,grmt->rqt",
        onehot.reshape(groups, slots, block_count),
        received,
        precision=high,
        preferred_element_type=jnp.float32,
    ).reshape(part, ancestors, order)
    own = jnp.zeros((part, ancestors, order), jnp.float32)
    own = lax.dynamic_update_slice(own, jnp.transpose(rhs_anc, (2, 0, 1)), (0, 0, me * rows))
    total = sum(gather_pieces(own - summed))
    first = contract_last(diag_inv_anc[0], total[:, 0])
    second = contract_last(diag_inv_anc[1], total[:, 1]) - contract_last(coupled, total[:, 0])
    return (jnp.stack(solved)[None], jnp.stack([first, second]))


def solution(mesh):
    return jax.shard_map(
        on_device,
        mesh=mesh,
        in_specs=(
            P("leaf", None, "grp", None),
            P("leaf", None, "grp", None),
            P("leaf", None, "grp", None),
            P("leaf", "grp", None, None, None),
            P("leaf", "grp", None),
            P("leaf", "grp", None),
            P("leaf", "grp"),
            P(None, "grp", "leaf"),
            P(None, "grp", None),
            P(None, "grp", None),
        ),
        out_specs=(P("leaf", None, "grp", None), P(None, "grp", "leaf")),
        check_vma=False,
    )
```

time: 299 us -> 226 us (0.76)
  blocking collectives: 167 us -> 12.6 us
  starting transfers between devices: 11.2 us -> 45.9 us
  waiting for transfers between devices: 62.6 us -> 88 us
  local copies, waits for them, and re-layouts: 10.3 us -> 23.4 us
  matrix products: 23.7 us -> 32.3 us
    all_gather x11 -> x0, blocking collectives: 167 us -> none  [the longest x6 88.8 us: on_device(): lax.all_gather(residual, 'grp', axis=0, tiled=True)]
    ppermute x0 -> x33, waiting for transfers between devices: none -> 78.9 us  [send(): lax.ppermute(value, axis, [(i, (i + shift) % count) for i in range(count)])]
    unnamed x2, waiting for transfers between devices: 50.7 us -> 0.03 us
    ppermute x0 -> x33, starting transfers between devices: none -> 42.4 us  [send(): lax.ppermute(value, axis, [(i, (i + shift) % count) for i in range(count)])]
    unnamed x0 -> x1, blocking collectives: none -> 12.6 us
    dot_general x12 -> x41, matrix products: 23.7 us -> 32.3 us  [the longest x36 26.6 us: product(): jnp.dot(left, right, precision=high, preferred_element_type=jnp.float32)]
    all_to_all x2 -> x1, starting transfers between devices: 11.2 us -> 3.41 us  [on_device(): lax.all_to_all(terms, 'leaf', split_axis=0, concat_axis=0, tiled=True)]
    slice x3 -> x4, local copies, waits for them, and re-layouts: 1.79 us -> 9.39 us  [the longest x1 4.46 us: on_device(): owned = apply_rows(inverse_group[current], gather_pieces(residual))]
  transfers between devices with their start and end apart: 3 -> 36, of which waited for: 2 -> 16; matrix products, arithmetic and copies ran while one was open for 11% -> 25% of each run, Pallas kernels for 0% -> 0%
where the time goes in v1:
time: 226 us; the launch traced here: 225 us
  waiting for transfers between devices  88 us (39%)
  starting transfers between devices  45.9 us (20%)
  matrix products  32.3 us (14%)
  local copies, waits for them, and re-layouts  23.4 us (10%)
  between operations  16 us (7%)
  blocking collectives  12.6 us (6%)
  other arithmetic  6.71 us (3%)
    ppermute x33, waiting for transfers between devices, send(): lax.ppermute(value, axis, [(i, (i + shift) % count) for i in range(count)])  78.9 us
    ppermute x33, starting transfers between devices, send(): lax.ppermute(value, axis, [(i, (i + shift) % count) for i in range(count)])  42.4 us
    dot_general x36, matrix products, product(): jnp.dot(left, right, precision=high, preferred_element_type=jnp.float32)  26.6 us
    unnamed x1, blocking collectives  12.6 us
    all_to_all x1, waiting for transfers between devices, on_device(): lax.all_to_all(terms, 'leaf', split_axis=0, concat_axis=0, tiled=True)  9.07 us
    gather x4, local copies, waits for them, and re-layouts, in_order(): return stacked[owners].reshape(-1, pieces[0].shape[-1])  4.96 us
  transfers between devices with their start and end apart: 36, of which 16 were waited for; matrix products, arithmetic and copies ran while one was open for 25% of the time, Pallas kernels for 0%

profile of v1, /device:TPU:0, one launch (start us, length us, event | category | flops | bytes accessed | tf_op | source)
XLA Modules:
  0.0 224.9 jit_solution(6997982201854517148)
XLA Ops:
  7.2 1.7 slice_bitcast_fusion
  8.9 5.0 %collective-permute-start.2 = (f32[256,128]{1,0:T(8,128)}, f32[256,128]{1,0:T(8,128)}, u32[]{:S(2)}, u32[]{:S(2)}) collective-permute-start(f32[256,128]{1,0:T(8,128)} %slice_bitcast_fusion), channel_id=1, source_target_pairs={{0,3},{1,0},{2,1},{3,2},{4,7},{5,4},{6,5},{7,6},{8,11},{9,8},{10,9... | collective-permute-start | bytes 393224 | tf_op jit(solution)/shard_map/ppermute | solution.py:25
  15.9 2.9 %collective-permute-start.29 = (f32[256,128]{1,0:T(8,128)S(1)}, f32[256,128]{1,0:T(8,128)}, u32[]{:S(2)}, u32[]{:S(2)}) collective-permute-start(f32[256,128]{1,0:T(8,128)S(1)} %dynamic-slice_bitcast_fusion.1), channel_id=1, source_target_pairs={{0,3},{1,0},{2,1},{3,2},{4,7},{5,4},{6,5},{7,6},{8,11},{9,8},{10,9... | collective-permute-start | bytes 393224 | tf_op jit(solution)/shard_map/ppermute | solution.py:25
  19.4 4.5 %fusion.164 = (f32[1,1,256,1024]{3,2,1,0:T(8,128)}, f32[1,1,256,1024]{3,2,1,0:T(8,128)}, f32[1,1,256,1024]{3,2,1,0:T(8,128)}, f32[1,1,256,1024]{3,2,1,0:T(8,128)}) fusion(f32[1,4,256,1024]{3,2,1,0:T(8,128)} %param.11), kind=kLoop, calls=%fused_computation.208 | loop fusion | bytes 8388608 | tf_op jit(solution)/shard_map/slice | solution.py:98
  23.9 1.6 fusion.165
  26.2 3.2 %fusion.166 = (f32[1,256,1024]{2,1,0:T(8,128)}, f32[1,256,1024]{2,1,0:T(8,128)}) fusion(f32[2,256,1024]{2,1,0:T(8,128)} %param.18), kind=kLoop, calls=%fused_computation.210 | loop fusion | bytes 4194304 | tf_op jit(solution)/shard_map/slice | solution.py:128
  29.4 1.2 fusion.71
  30.6 1.9 fusion.29
  33.9 12.6 %all-reduce = f32[24]{0:T(128)S(1)} all-reduce(f32[24]{0:T(128)S(1)} %fusion.158), channel_id=1, replica_groups=mesh['leaf'=8,'grp'=4] {'leaf'}, use_global_device_ids=true, to_apply=%add | all-reduce | flops 24 | bytes 192
  47.6 1.5 collective-permute-start.28
  49.1 1.3 convolution_add_fusion.17
  50.4 2.7 %collective-permute-start.32 = (f32[256,128]{1,0:T(8,128)S(1)}, f32[256,128]{1,0:T(8,128)}, u32[]{:S(2)}, u32[]{:S(2)}) collective-permute-start(f32[256,128]{1,0:T(8,128)S(1)} %dynamic-slice_bitcast_fusion), channel_id=1, source_target_pairs={{0,3},{1,0},{2,1},{3,2},{4,7},{5,4},{6,5},{7,6},{8,11},{9,8},{10,9... | collective-permute-start | bytes 393224 | tf_op jit(solution)/shard_map/ppermute | solution.py:25
  53.1 1.3 fusion.67
  54.4 1.3 fusion.16
  55.7 1.2 collective-permute-start.31
  56.9 1.2 convolution_add_fusion.3
  58.1 3.0 %collective-permute-start.5 = (f32[256,128]{1,0:T(8,128)S(1)}, f32[256,128]{1,0:T(8,128)}, u32[]{:S(2)}, u32[]{:S(2)}) collective-permute-start(f32[256,128]{1,0:T(8,128)S(1)} %fusion.16), channel_id=1, source_target_pairs={{0,3},{1,0},{2,1},{3,2},{4,7},{5,4},{6,5},{7,6},{8,11},{9,8},{10,9... | collective-permute-start | bytes 393224 | tf_op jit(solution)/shard_map/ppermute | solution.py:25
  61.1 1.2 fusion.25
  63.7 1.3 fusion.63
  65.0 4.1 %collective-permute-done.3 = f32[256,128]{1,0:T(8,128)S(1)} collective-permute-done((f32[256,128]{1,0:T(8,128)S(1)}, f32[256,128]{1,0:T(8,128)S(1)}, u32[]{:S(2)}, u32[]{:S(2)}) %collective-permute-start.3) | collective-permute-done | bytes 131104 | tf_op jit(solution)/shard_map/ppermute | solution.py:25
  69.8 5.1 %collective-permute-start.4 = (f32[256,128]{1,0:T(8,128)S(1)}, f32[256,128]{1,0:T(8,128)S(1)}, u32[]{:S(2)}, u32[]{:S(2)}) collective-permute-start(f32[256,128]{1,0:T(8,128)S(1)} %fusion.16), channel_id=1, source_target_pairs={{0,2},{1,3},{2,0},{3,1},{4,6},{5,7},{6,4},{7,5},{8,10},{9,11},{10,... | collective-permute-start | bytes 393224 | tf_op jit(solution)/shard_map/ppermute | solution.py:25
  74.9 1.3 convolution_add_fusion.15
  76.2 1.4 fusion.59
  77.5 3.4 %collective-permute-done.4 = f32[256,128]{1,0:T(8,128)S(1)} collective-permute-done((f32[256,128]{1,0:T(8,128)S(1)}, f32[256,128]{1,0:T(8,128)S(1)}, u32[]{:S(2)}, u32[]{:S(2)}) %collective-permute-start.4) | collective-permute-done | bytes 131104 | tf_op jit(solution)/shard_map/ppermute | solution.py:25
  80.9 1.2 fusion.15
  82.2 2.0 collective-permute-start.6
  84.5 4.9 %collective-permute-done.6 = f32[256,128]{1,0:T(8,128)S(1)} collective-permute-done((f32[256,128]{1,0:T(8,128)S(1)}, f32[256,128]{1,0:T(8,128)S(1)}, u32[]{:S(2)}, u32[]{:S(2)}) %collective-permute-start.6) | collective-permute-done | bytes 131104 | tf_op jit(solution)/shard_map/ppermute | solution.py:25
  89.4 2.0 collective-permute-start.7
  92.1 5.9 %collective-permute-done.7 = f32[256,128]{1,0:T(8,128)S(1)} collective-permute-done((f32[256,128]{1,0:T(8,128)S(1)}, f32[256,128]{1,0:T(8,128)S(1)}, u32[]{:S(2)}, u32[]{:S(2)}) %collective-permute-start.7) | collective-permute-done | bytes 131104 | tf_op jit(solution)/shard_map/ppermute | solution.py:25
  98.2 1.8 collective-permute-start.11
  100.6 6.2 %collective-permute-done.9 = f32[256,128]{1,0:T(8,128)S(1)} collective-permute-done((f32[256,128]{1,0:T(8,128)S(1)}, f32[256,128]{1,0:T(8,128)S(1)}, u32[]{:S(2)}, u32[]{:S(2)}) %collective-permute-start.9) | collective-permute-done | bytes 131104 | tf_op jit(solution)/shard_map/ppermute | solution.py:25
  107.7 5.6 %collective-permute-done.10 = f32[256,128]{1,0:T(8,128)S(1)} collective-permute-done((f32[256,128]{1,0:T(8,128)S(1)}, f32[256,128]{1,0:T(8,128)S(1)}, u32[]{:S(2)}, u32[]{:S(2)}) %collective-permute-start.10) | collective-permute-done | bytes 131104 | tf_op jit(solution)/shard_map/ppermute | solution.py:25
  113.7 1.7 collective-permute-start.14
  116.0 7.5 %collective-permute-done.12 = f32[256,128]{1,0:T(8,128)S(1)} collective-permute-done((f32[256,128]{1,0:T(8,128)S(1)}, f32[256,128]{1,0:T(8,128)S(1)}, u32[]{:S(2)}, u32[]{:S(2)}) %collective-permute-start.12) | collective-permute-done | bytes 131104 | tf_op jit(solution)/shard_map/ppermute | solution.py:25
  124.2 7.3 %collective-permute-done.13 = f32[256,128]{1,0:T(8,128)S(1)} collective-permute-done((f32[256,128]{1,0:T(8,128)S(1)}, f32[256,128]{1,0:T(8,128)S(1)}, u32[]{:S(2)}, u32[]{:S(2)}) %collective-permute-start.13) | collective-permute-done | bytes 131104 | tf_op jit(solution)/shard_map/ppermute | solution.py:25
  131.8 2.0 collective-permute-start.15
  134.1 4.6 %collective-permute-done.15 = f32[256,128]{1,0:T(8,128)S(1)} collective-permute-done((f32[256,128]{1,0:T(8,128)S(1)}, f32[256,128]{1,0:T(8,128)S(1)}, u32[]{:S(2)}, u32[]{:S(2)}) %collective-permute-start.15) | collective-permute-done | bytes 131104 | tf_op jit(solution)/shard_map/ppermute | solution.py:25
  138.7 1.1 collective-permute-start.16
  140.4 5.7 %collective-permute-done.16 = f32[256,128]{1,0:T(8,128)S(1)} collective-permute-done((f32[256,128]{1,0:T(8,128)S(1)}, f32[256,128]{1,0:T(8,128)S(1)}, u32[]{:S(2)}, u32[]{:S(2)}) %collective-permute-start.16) | collective-permute-done | bytes 131104 | tf_op jit(solution)/shard_map/ppermute | solution.py:25
  146.3 1.7 collective-permute-start.20
  148.7 7.3 %collective-permute-done.18 = f32[256,128]{1,0:T(8,128)S(1)} collective-permute-done((f32[256,128]{1,0:T(8,128)S(1)}, f32[256,128]{1,0:T(8,128)S(1)}, u32[]{:S(2)}, u32[]{:S(2)}) %collective-permute-start.18) | collective-permute-done | bytes 131104 | tf_op jit(solution)/shard_map/ppermute | solution.py:25
  156.5 5.3 %collective-permute-done.19 = f32[256,128]{1,0:T(8,128)S(1)} collective-permute-done((f32[256,128]{1,0:T(8,128)S(1)}, f32[256,128]{1,0:T(8,128)S(1)}, u32[]{:S(2)}, u32[]{:S(2)}) %collective-permute-start.19) | collective-permute-done | bytes 131104 | tf_op jit(solution)/shard_map/ppermute | solution.py:25
  162.1 1.4 collective-permute-start.23
  163.5 2.1 fusion.24
  166.2 1.6 gather_fusion.1
  167.8 1.4 gather_fusion
  169.1 1.2 fusion.77
  170.4 1.1 collective-permute-start.21
  171.5 1.3 convolution_add_fusion.1
  172.7 1.3 fusion.73
  174.0 1.9 fusion.5
  176.0 1.4 collective-permute-done.21
  178.0 1.1 pad_maximum_fusion.5
  179.1 1.4 gather_fusion.3
  180.5 2.7 %pad_maximum_fusion = f32[4,1024,128]{2,1,0:T(8,128)} fusion(f32[1,1024,128]{2,1,0:T(8,128)} %bitcast.227, f32[1,1024,128]{2,1,0:T(8,128)S(1)} %bitcast.224, f32[1,1024,128]{2,1,0:T(8,128)S(1)} %bitcast.225, f32[1,1024,128]{2,1,0:T(8,128)} %bitcast.226), kind=kLoop, calls=%fused_computation.5 | loop fusion | flops 1572864 | bytes 4194304 | tf_op jit(solution)/shard_map/stack | solution.py:105
  183.2 2.3 %gather_fusion.4 = f32[3,1024,128]{2,1,0:T(8,128)S(1)} fusion(f32[4,1024,128]{2,1,0:T(8,128)} %pad_maximum_fusion, s32[1024]{0:T(1024)S(1)} %pad_clamp_fusion), kind=kCustom, calls=%fused_computation.4 | custom fusion | bytes 3145740 | tf_op jit(solution)/shard_map/gather | solution.py:105
  185.5 1.4 fusion.2
  187.8 3.4 %all-to-all-start = ((f32[128,3,128]{2,1,0:T(4,128)}), f32[128,3,128]{2,1,0:T(4,128)S(1)}, u32[]{:S(2)}, u32[]{:S(2)}) async-start(f32[128,3,128]{2,1,0:T(4,128)} %copy.25), calls=%async_computation | async-start | bytes 524288 | tf_op jit(solution)/shard_map/all_to_all | solution.py:109
  191.3 9.1 %all-to-all-done = f32[128,3,128]{2,1,0:T(4,128)S(1)} async-done(((f32[128,3,128]{2,1,0:T(4,128)}), f32[128,3,128]{2,1,0:T(4,128)S(1)}, u32[]{:S(2)}, u32[]{:S(2)}) %all-to-all-start) | async-done | bytes 196640 | tf_op jit(solution)/shard_map/all_to_all | solution.py:109
  201.0 2.7 %collective-permute-start.25 = (f32[16,2,1024]{2,1,0:T(2,128)S(1)}, f32[16,2,1024]{2,1,0:T(2,128)S(1)}, u32[]{:S(2)}, u32[]{:S(2)}) collective-permute-start(f32[16,2,1024]{2,1,0:T(2,128)S(1)} %sub.26), channel_id=1, source_target_pairs={{0,2},{1,3},{2,0},{3,1},{4,6},{5,7},{6,4},{7,5},{8,10},{9,11},{10,... | collective-permute-start | bytes 393224 | tf_op jit(solution)/shard_map/ppermute | solution.py:25
  203.6 4.5 %collective-permute-done.26 = f32[16,2,1024]{2,1,0:T(2,128)S(1)} collective-permute-done((f32[16,2,1024]{2,1,0:T(2,128)S(1)}, f32[16,2,1024]{2,1,0:T(2,128)S(1)}, u32[]{:S(2)}, u32[]{:S(2)}) %collective-permute-start.26) | collective-permute-done | bytes 131104 | tf_op jit(solution)/shard_map/ppermute | solution.py:25
  208.2 5.0 %collective-permute-done.25 = f32[16,2,1024]{2,1,0:T(2,128)S(1)} collective-permute-done((f32[16,2,1024]{2,1,0:T(2,128)S(1)}, f32[16,2,1024]{2,1,0:T(2,128)S(1)}, u32[]{:S(2)}, u32[]{:S(2)}) %collective-permute-start.25) | collective-permute-done | bytes 131104 | tf_op jit(solution)/shard_map/ppermute | solution.py:25
  213.3 1.7 convolution_bitcast_fusion.2
  215.7 1.7 fusion.17
  (117 shorter events, 17.8 us)
Async XLA Ops:
  7.2 178.3 %copy-start = (f32[1,1,3,128,1024]{4,3,2,1,0:T(8,128)S(1)}, f32[1,1,3,128,1024]{4,3,2,1,0:T(8,128)}, u32[]{:S(2)}) copy-start(f32[1,1,3,128,1024]{4,3,2,1,0:T(8,128)} %param.13) | copy-start | bytes 4718596
  7.2 162.0 %all-gather.3.cloned.1.call-start = ((), (), s32[]{:S(2)}) async-start(), calls=%async_computation.1 | async-start | bytes 1179648 | tf_op jit(solution)/shard_map/all_gather | solution.py:83
  8.9 41.5 %collective-permute-start.2 = (f32[256,128]{1,0:T(8,128)}, f32[256,128]{1,0:T(8,128)}, u32[]{:S(2)}, u32[]{:S(2)}) collective-permute-start(f32[256,128]{1,0:T(8,128)} %slice_bitcast_fusion), channel_id=1, source_target_pairs={{0,3},{1,0},{2,1},{3,2},{4,7},{5,4},{6,5},{7,6},{8,11},{9,8},{10,9... | collective-permute-start | bytes 393224 | tf_op jit(solution)/shard_map/ppermute | solution.py:25
  14.0 33.7 %collective-permute-start = (f32[256,128]{1,0:T(8,128)}, f32[256,128]{1,0:T(8,128)}, u32[]{:S(2)}, u32[]{:S(2)}) collective-permute-start(f32[256,128]{1,0:T(8,128)} %slice_bitcast_fusion), channel_id=1, source_target_pairs={{0,1},{1,2},{2,3},{3,0},{4,5},{5,6},{6,7},{7,4},{8,9},{9,10},{10,1... | collective-permute-start | bytes 393224 | tf_op jit(solution)/shard_map/ppermute | solution.py:25
  14.0 40.4 %collective-permute-start.1 = (f32[256,128]{1,0:T(8,128)}, f32[256,128]{1,0:T(8,128)}, u32[]{:S(2)}, u32[]{:S(2)}) collective-permute-start(f32[256,128]{1,0:T(8,128)} %slice_bitcast_fusion), channel_id=1, source_target_pairs={{0,2},{1,3},{2,0},{3,1},{4,6},{5,7},{6,4},{7,5},{8,10},{9,11},{10,... | collective-permute-start | bytes 393224 | tf_op jit(solution)/shard_map/ppermute | solution.py:25
  15.9 42.2 %collective-permute-start.29 = (f32[256,128]{1,0:T(8,128)S(1)}, f32[256,128]{1,0:T(8,128)}, u32[]{:S(2)}, u32[]{:S(2)}) collective-permute-start(f32[256,128]{1,0:T(8,128)S(1)} %dynamic-slice_bitcast_fusion.1), channel_id=1, source_target_pairs={{0,3},{1,0},{2,1},{3,2},{4,7},{5,4},{6,5},{7,6},{8,11},{9,8},{10,9... | collective-permute-start | bytes 393224 | tf_op jit(solution)/shard_map/ppermute | solution.py:25
  18.7 37.0 %collective-permute-start.27 = (f32[256,128]{1,0:T(8,128)S(1)}, f32[256,128]{1,0:T(8,128)}, u32[]{:S(2)}, u32[]{:S(2)}) collective-permute-start(f32[256,128]{1,0:T(8,128)S(1)} %dynamic-slice_bitcast_fusion.1), channel_id=1, source_target_pairs={{0,1},{1,2},{2,3},{3,0},{4,5},{5,6},{6,7},{7,4},{8,9},{9,10},{10,1... | collective-permute-start | bytes 393224 | tf_op jit(solution)/shard_map/ppermute | solution.py:25
  19.4 4.5 %copy-start.7 = (f32[1,3,256,1024]{3,2,1,0:T(8,128)S(1)}, f32[1,3,256,1024]{3,2,1,0:T(8,128)}, u32[]{:S(2)}) copy-start(f32[1,3,256,1024]{3,2,1,0:T(8,128)} %param.12) | copy-start | bytes 9437188
  23.9 1.6 copy-start.15
  26.2 3.2 %copy-start.8 = (f32[1,4,256,128]{3,2,1,0:T(8,128)S(1)}, f32[1,4,256,128]{3,2,1,0:T(8,128)}, u32[]{:S(2)}) copy-start(f32[1,4,256,128]{3,2,1,0:T(8,128)} %param.10) | copy-start | bytes 1572868
  26.2 6.3 %copy-start.16 = (u32[32]{0:T(128)S(1)}, u32[32]{0:T(128)}, u32[]{:S(2)}) copy-start(u32[32]{0:T(128)} %constant.92) | copy-start | bytes 388
  26.2 7.6 %copy-start.14 = (s32[1,1,3]{2,1,0:T(1,128)S(1)}, s32[1,1,3]{2,1,0:T(1,128)}, u32[]{:S(2)}) copy-start(s32[1,1,3]{2,1,0:T(1,128)} %param.14) | copy-start | bytes 40
  46.6 10.3 %copy-start.3 = (f32[1,256,1024]{2,1,0:T(8,128)S(1)}, f32[1,256,1024]{2,1,0:T(8,128)}, u32[]{:S(2)}) copy-start(f32[1,256,1024]{2,1,0:T(8,128)} %get-tuple-element.9) | copy-start | bytes 3145732
  46.6 10.3 %copy-start.9 = (f32[256,128]{1,0:T(8,128)S(1)}, f32[256,128]{1,0:T(8,128)}, u32[]{:S(2)}) copy-start(f32[256,128]{1,0:T(8,128)} %fusion.29) | copy-start | bytes 393220
  47.6 14.6 %collective-permute-start.28 = (f32[256,128]{1,0:T(8,128)S(1)}, f32[256,128]{1,0:T(8,128)S(1)}, u32[]{:S(2)}, u32[]{:S(2)}) collective-permute-start(f32[256,128]{1,0:T(8,128)S(1)} %dynamic-slice_bitcast_fusion.1), channel_id=1, source_target_pairs={{0,2},{1,3},{2,0},{3,1},{4,6},{5,7},{6,4},{7,5},{8,10},{9,11},{10,... | collective-permute-start | bytes 393224 | tf_op jit(solution)/shard_map/ppermute | solution.py:25
  50.4 122.3 %collective-permute-start.32 = (f32[256,128]{1,0:T(8,128)S(1)}, f32[256,128]{1,0:T(8,128)}, u32[]{:S(2)}, u32[]{:S(2)}) collective-permute-start(f32[256,128]{1,0:T(8,128)S(1)} %dynamic-slice_bitcast_fusion), channel_id=1, source_target_pairs={{0,3},{1,0},{2,1},{3,2},{4,7},{5,4},{6,5},{7,6},{8,11},{9,8},{10,9... | collective-permute-start | bytes 393224 | tf_op jit(solution)/shard_map/ppermute | solution.py:25
  54.4 116.0 %collective-permute-start.30 = (f32[256,128]{1,0:T(8,128)S(1)}, f32[256,128]{1,0:T(8,128)}, u32[]{:S(2)}, u32[]{:S(2)}) collective-permute-start(f32[256,128]{1,0:T(8,128)S(1)} %dynamic-slice_bitcast_fusion), channel_id=1, source_target_pairs={{0,1},{1,2},{2,3},{3,0},{4,5},{5,6},{6,7},{7,4},{8,9},{9,10},{10,1... | collective-permute-start | bytes 393224 | tf_op jit(solution)/shard_map/ppermute | solution.py:25
  55.7 118.3 %collective-permute-start.31 = (f32[256,128]{1,0:T(8,128)S(1)}, f32[256,128]{1,0:T(8,128)}, u32[]{:S(2)}, u32[]{:S(2)}) collective-permute-start(f32[256,128]{1,0:T(8,128)S(1)} %dynamic-slice_bitcast_fusion), channel_id=1, source_target_pairs={{0,2},{1,3},{2,0},{3,1},{4,6},{5,7},{6,4},{7,5},{8,10},{9,11},{10,... | collective-permute-start | bytes 393224 | tf_op jit(solution)/shard_map/ppermute | solution.py:25
  58.1 18.0 %collective-permute-start.5 = (f32[256,128]{1,0:T(8,128)S(1)}, f32[256,128]{1,0:T(8,128)}, u32[]{:S(2)}, u32[]{:S(2)}) collective-permute-start(f32[256,128]{1,0:T(8,128)S(1)} %fusion.16), channel_id=1, source_target_pairs={{0,3},{1,0},{2,1},{3,2},{4,7},{5,4},{6,5},{7,6},{8,11},{9,8},{10,9... | collective-permute-start | bytes 393224 | tf_op jit(solution)/shard_map/ppermute | solution.py:25
  62.3 6.8 %collective-permute-start.3 = (f32[256,128]{1,0:T(8,128)S(1)}, f32[256,128]{1,0:T(8,128)S(1)}, u32[]{:S(2)}, u32[]{:S(2)}) collective-permute-start(f32[256,128]{1,0:T(8,128)S(1)} %fusion.16), channel_id=1, source_target_pairs={{0,1},{1,2},{2,3},{3,0},{4,5},{5,6},{6,7},{7,4},{8,9},{9,10},{10,1... | collective-permute-start | bytes 393224 | tf_op jit(solution)/shard_map/ppermute | solution.py:25
  63.6 152.0 %all-gather.5.cloned.1.call-start = ((), (), s32[]{:S(2)}) async-start(), calls=%async_computation.2 | async-start | bytes 1179648 | tf_op jit(solution)/shard_map/all_gather | solution.py:85
  63.7 20.6 %copy-start.6 = (f32[1,1,256,1024]{3,2,1,0:T(8,128)S(1)}, f32[1,1,256,1024]{3,2,1,0:T(8,128)}, u32[]{:S(2)}) copy-start(f32[1,1,256,1024]{3,2,1,0:T(8,128)} %get-tuple-element.3) | copy-start | bytes 3145732
  69.1 0.7 copy-start.10
  69.8 11.1 %collective-permute-start.4 = (f32[256,128]{1,0:T(8,128)S(1)}, f32[256,128]{1,0:T(8,128)S(1)}, u32[]{:S(2)}, u32[]{:S(2)}) collective-permute-start(f32[256,128]{1,0:T(8,128)S(1)} %fusion.16), channel_id=1, source_target_pairs={{0,2},{1,3},{2,0},{3,1},{4,6},{5,7},{6,4},{7,5},{8,10},{9,11},{10,... | collective-permute-start | bytes 393224 | tf_op jit(solution)/shard_map/ppermute | solution.py:25
  76.1 24.2 %copy-start.2 = (f32[1,1,256,1024]{3,2,1,0:T(8,128)S(1)}, f32[1,1,256,1024]{3,2,1,0:T(8,128)}, u32[]{:S(2)}) copy-start(f32[1,1,256,1024]{3,2,1,0:T(8,128)} %get-tuple-element.8) | copy-start | bytes 3145732
  82.2 9.6 %collective-permute-start.8 = (f32[256,128]{1,0:T(8,128)S(1)}, f32[256,128]{1,0:T(8,128)S(1)}, u32[]{:S(2)}, u32[]{:S(2)}) collective-permute-start(f32[256,128]{1,0:T(8,128)S(1)} %fusion.15), channel_id=1, source_target_pairs={{0,3},{1,0},{2,1},{3,2},{4,7},{5,4},{6,5},{7,6},{8,11},{9,8},{10,9... | collective-permute-start | bytes 393224 | tf_op jit(solution)/shard_map/ppermute | solution.py:25
  82.2 7.2 %collective-permute-start.6 = (f32[256,128]{1,0:T(8,128)S(1)}, f32[256,128]{1,0:T(8,128)S(1)}, u32[]{:S(2)}, u32[]{:S(2)}) collective-permute-start(f32[256,128]{1,0:T(8,128)S(1)} %fusion.15), channel_id=1, source_target_pairs={{0,1},{1,2},{2,3},{3,0},{4,5},{5,6},{6,7},{7,4},{8,9},{9,10},{10,1... | collective-permute-start | bytes 393224 | tf_op jit(solution)/shard_map/ppermute | solution.py:25
  89.4 8.5 %collective-permute-start.7 = (f32[256,128]{1,0:T(8,128)S(1)}, f32[256,128]{1,0:T(8,128)S(1)}, u32[]{:S(2)}, u32[]{:S(2)}) collective-permute-start(f32[256,128]{1,0:T(8,128)S(1)} %fusion.15), channel_id=1, source_target_pairs={{0,2},{1,3},{2,0},{3,1},{4,6},{5,7},{6,4},{7,5},{8,10},{9,11},{10,... | collective-permute-start | bytes 393224 | tf_op jit(solution)/shard_map/ppermute | solution.py:25
  91.7 24.0 %copy-start.5 = (f32[1,1,256,1024]{3,2,1,0:T(8,128)S(1)}, f32[1,1,256,1024]{3,2,1,0:T(8,128)}, u32[]{:S(2)}) copy-start(f32[1,1,256,1024]{3,2,1,0:T(8,128)} %get-tuple-element.5) | copy-start | bytes 3145732
  98.2 9.2 %collective-permute-start.11 = (f32[256,128]{1,0:T(8,128)S(1)}, f32[256,128]{1,0:T(8,128)S(1)}, u32[]{:S(2)}, u32[]{:S(2)}) collective-permute-start(f32[256,128]{1,0:T(8,128)S(1)} %fusion.13), channel_id=1, source_target_pairs={{0,3},{1,0},{2,1},{3,2},{4,7},{5,4},{6,5},{7,6},{8,11},{9,8},{10,9... | collective-permute-start | bytes 393224 | tf_op jit(solution)/shard_map/ppermute | solution.py:25
  100.0 6.8 %collective-permute-start.9 = (f32[256,128]{1,0:T(8,128)S(1)}, f32[256,128]{1,0:T(8,128)S(1)}, u32[]{:S(2)}, u32[]{:S(2)}) collective-permute-start(f32[256,128]{1,0:T(8,128)S(1)} %fusion.13), channel_id=1, source_target_pairs={{0,1},{1,2},{2,3},{3,0},{4,5},{5,6},{6,7},{7,4},{8,9},{9,10},{10,1... | collective-permute-start | bytes 393224 | tf_op jit(solution)/shard_map/ppermute | solution.py:25
  106.8 6.6 %collective-permute-start.10 = (f32[256,128]{1,0:T(8,128)S(1)}, f32[256,128]{1,0:T(8,128)S(1)}, u32[]{:S(2)}, u32[]{:S(2)}) collective-permute-start(f32[256,128]{1,0:T(8,128)S(1)} %fusion.13), channel_id=1, source_target_pairs={{0,2},{1,3},{2,0},{3,1},{4,6},{5,7},{6,4},{7,5},{8,10},{9,11},{10,... | collective-permute-start | bytes 393224 | tf_op jit(solution)/shard_map/ppermute | solution.py:25
  113.7 10.2 %collective-permute-start.14 = (f32[256,128]{1,0:T(8,128)S(1)}, f32[256,128]{1,0:T(8,128)S(1)}, u32[]{:S(2)}, u32[]{:S(2)}) collective-permute-start(f32[256,128]{1,0:T(8,128)S(1)} %fusion.12), channel_id=1, source_target_pairs={{0,3},{1,0},{2,1},{3,2},{4,7},{5,4},{6,5},{7,6},{8,11},{9,8},{10,9... | collective-permute-start | bytes 393224 | tf_op jit(solution)/shard_map/ppermute | solution.py:25
  115.4 8.2 %collective-permute-start.12 = (f32[256,128]{1,0:T(8,128)S(1)}, f32[256,128]{1,0:T(8,128)S(1)}, u32[]{:S(2)}, u32[]{:S(2)}) collective-permute-start(f32[256,128]{1,0:T(8,128)S(1)} %fusion.12), channel_id=1, source_target_pairs={{0,1},{1,2},{2,3},{3,0},{4,5},{5,6},{6,7},{7,4},{8,9},{9,10},{10,1... | collective-permute-start | bytes 393224 | tf_op jit(solution)/shard_map/ppermute | solution.py:25
  123.6 7.9 %collective-permute-start.13 = (f32[256,128]{1,0:T(8,128)S(1)}, f32[256,128]{1,0:T(8,128)S(1)}, u32[]{:S(2)}, u32[]{:S(2)}) collective-permute-start(f32[256,128]{1,0:T(8,128)S(1)} %fusion.12), channel_id=1, source_target_pairs={{0,2},{1,3},{2,0},{3,1},{4,6},{5,7},{6,4},{7,5},{8,10},{9,11},{10,... | collective-permute-start | bytes 393224 | tf_op jit(solution)/shard_map/ppermute | solution.py:25
  123.8 24.6 %copy-start.4 = (f32[1,1,256,1024]{3,2,1,0:T(8,128)S(1)}, f32[1,1,256,1024]{3,2,1,0:T(8,128)}, u32[]{:S(2)}) copy-start(f32[1,1,256,1024]{3,2,1,0:T(8,128)} %get-tuple-element.2) | copy-start | bytes 3145732
  131.8 8.3 %collective-permute-start.17 = (f32[256,128]{1,0:T(8,128)S(1)}, f32[256,128]{1,0:T(8,128)S(1)}, u32[]{:S(2)}, u32[]{:S(2)}) collective-permute-start(f32[256,128]{1,0:T(8,128)S(1)} %fusion.10), channel_id=1, source_target_pairs={{0,3},{1,0},{2,1},{3,2},{4,7},{5,4},{6,5},{7,6},{8,11},{9,8},{10,9... | collective-permute-start | bytes 393224 | tf_op jit(solution)/shard_map/ppermute | solution.py:25
  131.8 6.9 %collective-permute-start.15 = (f32[256,128]{1,0:T(8,128)S(1)}, f32[256,128]{1,0:T(8,128)S(1)}, u32[]{:S(2)}, u32[]{:S(2)}) collective-permute-start(f32[256,128]{1,0:T(8,128)S(1)} %fusion.10), channel_id=1, source_target_pairs={{0,1},{1,2},{2,3},{3,0},{4,5},{5,6},{6,7},{7,4},{8,9},{9,10},{10,1... | collective-permute-start | bytes 393224 | tf_op jit(solution)/shard_map/ppermute | solution.py:25
  138.7 7.3 %collective-permute-start.16 = (f32[256,128]{1,0:T(8,128)S(1)}, f32[256,128]{1,0:T(8,128)S(1)}, u32[]{:S(2)}, u32[]{:S(2)}) collective-permute-start(f32[256,128]{1,0:T(8,128)S(1)} %fusion.10), channel_id=1, source_target_pairs={{0,2},{1,3},{2,0},{3,1},{4,6},{5,7},{6,4},{7,5},{8,10},{9,11},{10,... | collective-permute-start | bytes 393224 | tf_op jit(solution)/shard_map/ppermute | solution.py:25
  140.1 23.4 %copy-start.11 = (f32[256,128]{1,0:T(8,128)S(1)}, f32[256,128]{1,0:T(8,128)}, u32[]{:S(2)}) copy-start(f32[256,128]{1,0:T(8,128)} %copy-done.10) | copy-start | bytes 393220
  146.3 9.9 %collective-permute-start.20 = (f32[256,128]{1,0:T(8,128)S(1)}, f32[256,128]{1,0:T(8,128)S(1)}, u32[]{:S(2)}, u32[]{:S(2)}) collective-permute-start(f32[256,128]{1,0:T(8,128)S(1)} %fusion.9), channel_id=1, source_target_pairs={{0,3},{1,0},{2,1},{3,2},{4,7},{5,4},{6,5},{7,6},{8,11},{9,8},{10,9... | collective-permute-start | bytes 393224 | tf_op jit(solution)/shard_map/ppermute | solution.py:25
  148.0 8.0 %collective-permute-start.18 = (f32[256,128]{1,0:T(8,128)S(1)}, f32[256,128]{1,0:T(8,128)S(1)}, u32[]{:S(2)}, u32[]{:S(2)}) collective-permute-start(f32[256,128]{1,0:T(8,128)S(1)} %fusion.9), channel_id=1, source_target_pairs={{0,1},{1,2},{2,3},{3,0},{4,5},{5,6},{6,7},{7,4},{8,9},{9,10},{10,1... | collective-permute-start | bytes 393224 | tf_op jit(solution)/shard_map/ppermute | solution.py:25
  155.9 5.9 %collective-permute-start.19 = (f32[256,128]{1,0:T(8,128)S(1)}, f32[256,128]{1,0:T(8,128)S(1)}, u32[]{:S(2)}, u32[]{:S(2)}) collective-permute-start(f32[256,128]{1,0:T(8,128)S(1)} %fusion.9), channel_id=1, source_target_pairs={{0,2},{1,3},{2,0},{3,1},{4,6},{5,7},{6,4},{7,5},{8,10},{9,11},{10,... | collective-permute-start | bytes 393224 | tf_op jit(solution)/shard_map/ppermute | solution.py:25
  162.1 13.9 %collective-permute-start.23 = (f32[256,128]{1,0:T(8,128)S(1)}, f32[256,128]{1,0:T(8,128)}, u32[]{:S(2)}, u32[]{:S(2)}) collective-permute-start(f32[256,128]{1,0:T(8,128)S(1)} %fusion.7), channel_id=1, source_target_pairs={{0,3},{1,0},{2,1},{3,2},{4,7},{5,4},{6,5},{7,6},{8,11},{9,8},{10,9... | collective-permute-start | bytes 393224 | tf_op jit(solution)/shard_map/ppermute | solution.py:25
  163.4 12.6 %collective-permute-start.22 = (f32[256,128]{1,0:T(8,128)S(1)}, f32[256,128]{1,0:T(8,128)}, u32[]{:S(2)}, u32[]{:S(2)}) collective-permute-start(f32[256,128]{1,0:T(8,128)S(1)} %fusion.7), channel_id=1, source_target_pairs={{0,2},{1,3},{2,0},{3,1},{4,6},{5,7},{6,4},{7,5},{8,10},{9,11},{10,... | collective-permute-start | bytes 393224 | tf_op jit(solution)/shard_map/ppermute | solution.py:25
  170.4 7.0 %collective-permute-start.21 = (f32[256,128]{1,0:T(8,128)S(1)}, f32[256,128]{1,0:T(8,128)S(1)}, u32[]{:S(2)}, u32[]{:S(2)}) collective-permute-start(f32[256,128]{1,0:T(8,128)S(1)} %fusion.7), channel_id=1, source_target_pairs={{0,1},{1,2},{2,3},{3,0},{4,5},{5,6},{6,7},{7,4},{8,9},{9,10},{10,1... | collective-permute-start | bytes 393224 | tf_op jit(solution)/shard_map/ppermute | solution.py:25
  177.4 0.7 copy-start.12
  185.5 5.8 %copy-start.13 = (f32[2,256,16]{1,2,0:T(8,128)S(1)}, f32[2,256,16]{1,2,0:T(8,128)}, u32[]{:S(2)}) copy-start(f32[2,256,16]{1,2,0:T(8,128)} %param.17) | copy-start | bytes 98308
  187.8 12.6 %all-to-all-start = ((f32[128,3,128]{2,1,0:T(4,128)}), f32[128,3,128]{2,1,0:T(4,128)S(1)}, u32[]{:S(2)}, u32[]{:S(2)}) async-start(f32[128,3,128]{2,1,0:T(4,128)} %copy.25), calls=%async_computation | async-start | bytes 524288 | tf_op jit(solution)/shard_map/all_to_all | solution.py:109
  200.8 14.3 %copy-start.1 = (f32[2,256,1024]{2,1,0:T(8,128)S(1)}, f32[2,256,1024]{2,1,0:T(8,128)}, u32[]{:S(2)}) copy-start(f32[2,256,1024]{2,1,0:T(8,128)} %param.18) | copy-start | bytes 6291460
  200.9 7.3 %collective-permute-start.26 = (f32[16,2,1024]{2,1,0:T(2,128)S(1)}, f32[16,2,1024]{2,1,0:T(2,128)S(1)}, u32[]{:S(2)}, u32[]{:S(2)}) collective-permute-start(f32[16,2,1024]{2,1,0:T(2,128)S(1)} %sub.26), channel_id=1, source_target_pairs={{0,3},{1,0},{2,1},{3,2},{4,7},{5,4},{6,5},{7,6},{8,11},{9,8},{10,9... | collective-permute-start | bytes 393224 | tf_op jit(solution)/shard_map/ppermute | solution.py:25
  201.0 12.2 %collective-permute-start.25 = (f32[16,2,1024]{2,1,0:T(2,128)S(1)}, f32[16,2,1024]{2,1,0:T(2,128)S(1)}, u32[]{:S(2)}, u32[]{:S(2)}) collective-permute-start(f32[16,2,1024]{2,1,0:T(2,128)S(1)} %sub.26), channel_id=1, source_target_pairs={{0,2},{1,3},{2,0},{3,1},{4,6},{5,7},{6,4},{7,5},{8,10},{9,11},{10,... | collective-permute-start | bytes 393224 | tf_op jit(solution)/shard_map/ppermute | solution.py:25
  203.6 9.6 %collective-permute-start.24 = (f32[16,2,1024]{2,1,0:T(2,128)S(1)}, f32[16,2,1024]{2,1,0:T(2,128)S(1)}, u32[]{:S(2)}, u32[]{:S(2)}) collective-permute-start(f32[16,2,1024]{2,1,0:T(2,128)S(1)} %sub.26), channel_id=1, source_target_pairs={{0,1},{1,2},{2,3},{3,0},{4,5},{5,6},{6,7},{7,4},{8,9},{9,10},{10,1... | collective-permute-start | bytes 393224 | tf_op jit(solution)/shard_map/ppermute | solution.py:25
Sparse Core Ops, SparseCore 0:
  63.7 23.1 all-gather.2
  176.1 25.4 all-gather.4

commit v2 on v1

v2 whole, which is shorter than its diff:
```python
import jax
import jax.numpy as jnp
from jax import lax
from jax.sharding import PartitionSpec as P

high = lax.Precision.HIGH


def product(left, right):
    return jnp.dot(left, right, precision=high, preferred_element_type=jnp.float32)


def contract_last(left, right):
    return lax.dot_general(
        left,
        right,
        (((left.ndim - 1,), (right.ndim - 1,)), ((), ())),
        precision=high,
        preferred_element_type=jnp.float32,
    )


def ring_member(place, members):
    if place == 0:
        return 0
    return 2 * place - 1 if place <= members // 2 else 2 * (members - place)


def ring_place_of(member, members):
    return jnp.where(
        member % 2 == 1, (member + 1) // 2, jnp.where(member == 0, 0, members - member // 2)
    )


def ring_member_of(place, members):
    return jnp.where(place <= members // 2, jnp.maximum(2 * place - 1, 0), 2 * (members - place))


def ring_send(value, step):
    members = lax.axis_size("grp")
    pairs = [
        (ring_member(p, members), ring_member((p + step) % members, members))
        for p in range(members)
    ]
    return lax.ppermute(value, "grp", pairs)


def ring_owner(distance):
    members = lax.axis_size("grp")
    place = ring_place_of(lax.axis_index("grp"), members)
    return ring_member_of(lax.rem(place - distance + members, members), members)


def ring_gather(value):
    members = lax.axis_size("grp")
    rows = value.shape[0]
    half = rows // 2
    low, high_part = value[:half], value[half:]
    pieces = [(lax.axis_index("grp") * rows, value)]
    forward = [low, high_part]
    backward = [low, high_part]
    for distance in range(1, members // 2 + 1):
        last = 2 * distance == members
        ahead = ring_owner(distance) * rows
        behind = ring_owner(-distance) * rows
        if last:
            forward[0] = ring_send(forward[0], 1)
            backward[1] = ring_send(backward[1], -1)
            pieces.append((ahead, forward[0]))
            pieces.append((behind + half, backward[1]))
        else:
            forward[0] = ring_send(forward[0], 1)
            backward[1] = ring_send(backward[1], -1)
            forward[1] = ring_send(forward[1], 1)
            backward[0] = ring_send(backward[0], -1)
            pieces.append((ahead, forward[0]))
            pieces.append((behind + half, backward[1]))
            pieces.append((ahead + half, forward[1]))
            pieces.append((behind, backward[0]))
    return pieces


def apply_rows(matrix, pieces):
    total = None
    for offset, piece in pieces:
        columns = lax.dynamic_slice_in_dim(matrix, offset, piece.shape[0], 1)
        term = product(columns, piece)
        total = term if total is None else total + term
    return total


def send(value, axis, shift):
    count = lax.axis_size(axis)
    return lax.ppermute(value, axis, [(i, (i + shift) % count) for i in range(count)])


def apply_wide(matrix, portion):
    members = lax.axis_size("grp")
    me = lax.axis_index("grp")
    rows = portion.shape[-1]
    total = None
    for shift in range(members):
        piece = portion if shift == 0 else send(portion, "grp", shift)
        owner = lax.rem(me - shift + members, members)
        columns = lax.dynamic_slice_in_dim(matrix, owner * rows, rows, 1)
        term = contract_last(piece, columns)
        total = term if total is None else total + term
    return total


def assemble(pieces, order):
    whole = jnp.zeros((order, pieces[0][1].shape[1]), jnp.float32)
    for offset, piece in pieces:
        whole = lax.dynamic_update_slice_in_dim(whole, piece, offset, 0)
    return whole


def on_device(
    rhs_local,
    diag_inv_local,
    sub_local,
    tiles,
    tile_block,
    tile_source,
    tile_count,
    rhs_anc,
    diag_inv_anc,
    sub_anc,
):
    rhs_group = rhs_local[0]
    inverse_group = diag_inv_local[0]
    below_group = sub_local[0]
    supernodes = rhs_group.shape[0]
    order = inverse_group.shape[-1]
    rhs_count = rhs_group.shape[-1]
    members = lax.axis_size("grp")
    groups = lax.axis_size("leaf")
    me = lax.axis_index("grp")
    leaf = lax.axis_index("leaf")
    rows = order // members
    part = rhs_count // groups

    tiles_mine = tiles[0, 0]
    slots, tile_rows = tiles_mine.shape[:2]
    blocks = jnp.where(
        jnp.arange(slots, dtype=jnp.int32) < tile_count[0, 0], tile_block[0, 0], -1
    ).astype(jnp.float32)
    sources = tile_source[0, 0]

    solved = []
    residual = rhs_group[0]
    chosen = jnp.zeros((slots, order, rhs_count), jnp.float32)
    for current in range(supernodes):
        owned = apply_rows(inverse_group[current], ring_gather(residual))
        solved.append(owned)
        pieces = ring_gather(owned)
        if current + 1 < supernodes:
            residual = rhs_group[current + 1] - apply_rows(below_group[current], pieces)
            whole = assemble(pieces, order)
            chosen = jnp.where((sources == current)[:, None, None], whole[None], chosen)

    early = jnp.einsum(
        "mtk,mkr->rmt", tiles_mine, chosen, precision=high, preferred_element_type=jnp.float32
    ).reshape(rhs_count, slots * tile_rows)
    flat_tiles = tiles_mine.reshape(slots * tile_rows, order)
    late = None
    for offset, piece in pieces:
        columns = lax.dynamic_slice_in_dim(flat_tiles, offset, piece.shape[0], 1)
        term = lax.dot_general(
            piece,
            columns,
            (((0,), (1,)), ((), ())),
            precision=high,
            preferred_element_type=jnp.float32,
        )
        late = term if late is None else late + term
    is_late = jnp.repeat(sources == supernodes - 1, tile_rows)
    terms = jnp.where(is_late[None, :], late, early)
    tag = jnp.zeros((tile_rows,), jnp.float32).at[:slots].set(blocks)
    terms = jnp.concatenate(
        [terms, jnp.broadcast_to(tag[None, :], (rhs_count, tile_rows))], axis=1
    )

    received = [lax.dynamic_slice_in_dim(terms, leaf * part, part, 0)]
    for shift in range(1, groups):
        target = lax.rem(leaf + shift, groups)
        received.append(
            send(lax.dynamic_slice_in_dim(terms, target * part, part, 0), "leaf", shift)
        )
    received = jnp.stack(received)
    ancestors = rhs_anc.shape[0]
    block_count = ancestors * order // tile_rows
    width = slots * tile_rows
    onehot = (
        received[:, 0, width : width + slots, None]
        == jnp.arange(block_count, dtype=jnp.float32)[None, None, :]
    ).astype(jnp.float32)
    summed = jnp.einsum(
        "gmq,grmt->rqt",
        onehot,
        received[:, :, :width].reshape(groups, part, slots, tile_rows),
        precision=high,
        preferred_element_type=jnp.float32,
    ).reshape(part, ancestors, order)
    own = jnp.zeros((part, ancestors, order), jnp.float32)
    own = lax.dynamic_update_slice(own, jnp.transpose(rhs_anc, (2, 0, 1)), (0, 0, me * rows))
    share = own - summed

    first_share = share[:, 0]
    total = None
    for shift in range(members):
        target = lax.rem(me + shift, members)
        payload = [first_share] + [
            lax.dynamic_slice_in_dim(share[:, a], target * rows, rows, 1)
            for a in range(1, ancestors)
        ]
        payload = jnp.concatenate(payload, axis=1)
        payload = payload if shift == 0 else send(payload, "grp", shift)
        total = payload if total is None else total + payload
    solutions = [contract_last(total[:, :order], diag_inv_anc[0])]
    for ancestor in range(1, ancestors):
        begin = order + (ancestor - 1) * rows
        residual = total[:, begin : begin + rows] - apply_wide(sub_anc[ancestor - 1], solutions[-1])
        solutions.append(apply_wide(diag_inv_anc[ancestor], residual))
    solutions = jnp.stack([jnp.transpose(s) for s in solutions])
    return (jnp.stack(solved)[None], solutions)


def solution(mesh):
    return jax.shard_map(
        on_device,
        mesh=mesh,
        in_specs=(
            P("leaf", None, "grp", None),
            P("leaf", None, "grp", None),
            P("leaf", None, "grp", None),
            P("leaf", "grp", None, None, None),
            P("leaf", "grp", None),
            P("leaf", "grp", None),
            P("leaf", "grp"),
            P(None, "grp", "leaf"),
            P(None, "grp", None),
            P(None, "grp", None),
        ),
        out_specs=(P("leaf", None, "grp", None), P(None, "grp", "leaf")),
        check_vma=False,
    )
```

time: 226 us -> 183 us (0.81)
  starting transfers between devices: 45.9 us -> 91.8 us
  waiting for transfers between devices: 88 us -> 42.1 us
  between operations: 16 us -> 2.47 us
  blocking collectives: 12.6 us -> 0 us
  local copies, waits for them, and re-layouts: 23.4 us -> 13.9 us
  matrix products: 32.3 us -> 27.4 us
  other arithmetic: 6.71 us -> 4.3 us
    ppermute x33 -> x16, waiting for transfers between devices: 78.9 us -> 10.5 us  [send(): lax.ppermute(value, axis, [(i, (i + shift) % count) for i in range(count)])]
    ppermute x0 -> x48, starting transfers between devices: none -> 67.8 us  [ring_send(): return lax.ppermute(value, 'grp', pairs)]
    ppermute x0 -> x48, waiting for transfers between devices: none -> 31.6 us  [ring_send(): return lax.ppermute(value, 'grp', pairs)]
    ppermute x33 -> x16, starting transfers between devices: 42.4 us -> 24 us  [send(): lax.ppermute(value, axis, [(i, (i + shift) % count) for i in range(count)])]
    unnamed x1 -> x0, blocking collectives: 12.6 us -> none
    all_to_all x1 -> x0, waiting for transfers between devices: 9.07 us -> none  [on_device(): lax.all_to_all(terms, 'leaf', split_axis=0, concat_axis=0, tiled=True)]
    gather x5 -> x0, local copies, waits for them, and re-layouts: 7.24 us -> none  [the longest x4 4.96 us: in_order(): return stacked[owners].reshape(-1, pieces[0].shape[-1])]
    dot_general x36 -> x49, matrix products: 26.6 us -> 20.4 us  [product(): jnp.dot(left, right, precision=high, preferred_element_type=jnp.float32)]
  transfers between devices with their start and end apart: 36 -> 64, of which waited for: 16 -> 29; matrix products, arithmetic and copies ran while one was open for 25% -> 19% of each run, Pallas kernels for 0% -> 0%
where the time goes in v2:
time: 183 us; the launch traced here: 182 us
  starting transfers between devices  91.8 us (50%)
  waiting for transfers between devices  42.1 us (23%)
  matrix products  27.4 us (15%)
  local copies, waits for them, and re-layouts  13.9 us (8%)
  other arithmetic  4.3 us (2%)
  between operations  2.47 us (1%)
    ppermute x48, starting transfers between devices, ring_send(): return lax.ppermute(value, 'grp', pairs)  67.8 us
    ppermute x48, waiting for transfers between devices, ring_send(): return lax.ppermute(value, 'grp', pairs)  31.6 us
    ppermute x16, starting transfers between devices, send(): lax.ppermute(value, axis, [(i, (i + shift) % count) for i in range(count)])  24 us
    dot_general x49, matrix products, product(): jnp.dot(left, right, precision=high, preferred_element_type=jnp.float32)  20.4 us
    ppermute x16, waiting for transfers between devices, send(): lax.ppermute(value, axis, [(i, (i + shift) % count) for i in range(count)])  10.5 us
    slice x1, local copies, waits for them, and re-layouts, on_device(): owned = apply_rows(inverse_group[current], ring_gather(residual))  4.4 us
  transfers between devices with their start and end apart: 64, of which 29 were waited for; matrix products, arithmetic and copies ran while one was open for 19% of the time, Pallas kernels for 0%

profile of v2, /device:TPU:0, one launch (start us, length us, event | category | flops | bytes accessed | tf_op | source)
XLA Modules:
  0.0 182.0 jit_solution(4458990892205789997)
XLA Ops:
  0.6 1.7 slice_bitcast_fusion.2
  2.3 3.0 %collective-permute-start = (f32[128,128]{1,0:T(8,128)}, f32[128,128]{1,0:T(8,128)}, u32[]{:S(2)}, u32[]{:S(2)}) collective-permute-start(f32[128,128]{1,0:T(8,128)} %get-tuple-element.21), channel_id=1, source_target_pairs={{0,1},{1,3},{3,2},{2,0},{4,5},{5,7},{7,6},{6,4},{8,9},{9,11},{11,1... | collective-permute-start | bytes 196616 | tf_op jit(solution)/shard_map/ppermute | solution.py:45
  6.3 1.6 collective-permute-start.2
  7.9 1.3 collective-permute-start.1
  9.3 4.4 %fusion.285 = (f32[1,1,256,1024]{3,2,1,0:T(8,128)}, f32[1,1,256,1024]{3,2,1,0:T(8,128)}, f32[1,1,256,1024]{3,2,1,0:T(8,128)}, f32[1,1,256,1024]{3,2,1,0:T(8,128)}) fusion(f32[1,4,256,1024]{3,2,1,0:T(8,128)} %param.13), kind=kLoop, calls=%fused_computation.374 | loop fusion | bytes 8388608 | tf_op jit(solution)/shard_map/slice | solution.py:154
  13.7 3.6 %fusion.286 = (f32[1,1,256,1024]{3,2,1,0:T(8,128)S(1)}, f32[1,1,256,1024]{3,2,1,0:T(8,128)}, f32[1,1,256,1024]{3,2,1,0:T(8,128)}) fusion(f32[1,3,256,1024]{3,2,1,0:T(8,128)} %param.14), kind=kLoop, calls=%fused_computation.375 | loop fusion | bytes 6291456 | tf_op jit(solution)/shard_map/slice | solution.py:158
  18.5 1.2 fusion.74
  21.7 1.6 collective-permute-start.5
  24.9 1.2 fusion.160
  30.7 2.6 %collective-permute-start.6 = (f32[128,128]{1,0:T(8,128)S(1)}, f32[128,128]{1,0:T(8,128)S(1)}, u32[]{:S(2)}, u32[]{:S(2)}) collective-permute-start(f32[128,128]{1,0:T(8,128)S(1)} %get-tuple-element.44), channel_id=1, source_target_pairs={{0,1},{1,3},{3,2},{2,0},{4,5},{5,7},{7,6},{6,4},{8,9},{9,11},{11,1... | collective-permute-start | bytes 196616 | tf_op jit(solution)/shard_map/ppermute | solution.py:45
  33.7 1.6 collective-permute-start.8
  35.3 1.3 collective-permute-start.7
  37.0 1.6 collective-permute-start.10
  38.9 1.8 collective-permute-done.8
  42.6 4.0 %collective-permute-done.11 = f32[128,128]{1,0:T(8,128)S(1)} collective-permute-done((f32[128,128]{1,0:T(8,128)S(1)}, f32[128,128]{1,0:T(8,128)S(1)}, u32[]{:S(2)}, u32[]{:S(2)}) %collective-permute-start.11) | collective-permute-done | bytes 65568 | tf_op jit(solution)/shard_map/ppermute | solution.py:45
  47.0 2.3 %collective-permute-start.12 = (f32[128,128]{1,0:T(8,128)S(1)}, f32[128,128]{1,0:T(8,128)S(1)}, u32[]{:S(2)}, u32[]{:S(2)}) collective-permute-start(f32[128,128]{1,0:T(8,128)S(1)} %get-tuple-element.42), channel_id=1, source_target_pairs={{0,1},{1,3},{3,2},{2,0},{4,5},{5,7},{7,6},{6,4},{8,9},{9,11},{11,1... | collective-permute-start | bytes 196616 | tf_op jit(solution)/shard_map/ppermute | solution.py:45
  50.0 1.3 collective-permute-start.14
  51.3 1.6 collective-permute-start.13
  54.0 1.2 collective-permute-done.14
  55.9 2.2 %collective-permute-start.17 = (f32[128,128]{1,0:T(8,128)S(1)}, f32[128,128]{1,0:T(8,128)S(1)}, u32[]{:S(2)}, u32[]{:S(2)}) collective-permute-start(f32[128,128]{1,0:T(8,128)S(1)} %collective-permute-done.13), channel_id=1, source_target_pairs={{0,2},{1,0},{3,1},{2,3},{4,6},{5,4},{7,5},{6,7},{8,10},{9,8},{11,9... | collective-permute-start | bytes 196616 | tf_op jit(solution)/shard_map/ppermute | solution.py:45
  58.3 2.3 %collective-permute-done.17 = f32[128,128]{1,0:T(8,128)S(1)} collective-permute-done((f32[128,128]{1,0:T(8,128)S(1)}, f32[128,128]{1,0:T(8,128)S(1)}, u32[]{:S(2)}, u32[]{:S(2)}) %collective-permute-start.17) | collective-permute-done | bytes 65568 | tf_op jit(solution)/shard_map/ppermute | solution.py:45
  61.1 2.9 %collective-permute-start.18 = (f32[128,128]{1,0:T(8,128)S(1)}, f32[128,128]{1,0:T(8,128)S(1)}, u32[]{:S(2)}, u32[]{:S(2)}) collective-permute-start(f32[128,128]{1,0:T(8,128)S(1)} %get-tuple-element.40), channel_id=1, source_target_pairs={{0,1},{1,3},{3,2},{2,0},{4,5},{5,7},{7,6},{6,4},{8,9},{9,11},{11,1... | collective-permute-start | bytes 196616 | tf_op jit(solution)/shard_map/ppermute | solution.py:45
  64.6 1.4 collective-permute-start.20
  66.0 1.5 collective-permute-start.19
  68.8 1.2 collective-permute-done.20
  70.7 2.2 %collective-permute-start.23 = (f32[128,128]{1,0:T(8,128)S(1)}, f32[128,128]{1,0:T(8,128)S(1)}, u32[]{:S(2)}, u32[]{:S(2)}) collective-permute-start(f32[128,128]{1,0:T(8,128)S(1)} %collective-permute-done.19), channel_id=1, source_target_pairs={{0,2},{1,0},{3,1},{2,3},{4,6},{5,4},{7,5},{6,7},{8,10},{9,8},{11,9... | collective-permute-start | bytes 196616 | tf_op jit(solution)/shard_map/ppermute | solution.py:45
  73.1 2.5 %collective-permute-done.23 = f32[128,128]{1,0:T(8,128)S(1)} collective-permute-done((f32[128,128]{1,0:T(8,128)S(1)}, f32[128,128]{1,0:T(8,128)S(1)}, u32[]{:S(2)}, u32[]{:S(2)}) %collective-permute-start.23) | collective-permute-done | bytes 65568 | tf_op jit(solution)/shard_map/ppermute | solution.py:45
  76.1 2.3 %collective-permute-start.24 = (f32[128,128]{1,0:T(8,128)S(1)}, f32[128,128]{1,0:T(8,128)S(1)}, u32[]{:S(2)}, u32[]{:S(2)}) collective-permute-start(f32[128,128]{1,0:T(8,128)S(1)} %get-tuple-element.38), channel_id=1, source_target_pairs={{0,1},{1,3},{3,2},{2,0},{4,5},{5,7},{7,6},{6,4},{8,9},{9,11},{11,1... | collective-permute-start | bytes 196616 | tf_op jit(solution)/shard_map/ppermute | solution.py:45
  79.0 1.4 collective-permute-start.26
  80.4 1.6 collective-permute-start.25
  83.0 1.9 %collective-permute-done.26 = f32[128,128]{1,0:T(8,128)S(1)} collective-permute-done((f32[128,128]{1,0:T(8,128)S(1)}, f32[128,128]{1,0:T(8,128)S(1)}, u32[]{:S(2)}, u32[]{:S(2)}) %collective-permute-start.26) | collective-permute-done | bytes 65568 | tf_op jit(solution)/shard_map/ppermute | solution.py:45
  85.3 1.4 collective-permute-done.25
  88.1 3.5 %collective-permute-done.29 = f32[128,128]{1,0:T(8,128)S(1)} collective-permute-done((f32[128,128]{1,0:T(8,128)S(1)}, f32[128,128]{1,0:T(8,128)S(1)}, u32[]{:S(2)}, u32[]{:S(2)}) %collective-permute-start.29) | collective-permute-done | bytes 65568 | tf_op jit(solution)/shard_map/ppermute | solution.py:45
  92.1 1.6 collective-permute-start.30
  93.8 1.4 collective-permute-start.33
  95.8 2.3 %collective-permute-start.31 = (f32[128,128]{1,0:T(8,128)S(1)}, f32[128,128]{1,0:T(8,128)S(1)}, u32[]{:S(2)}, u32[]{:S(2)}) collective-permute-start(f32[128,128]{1,0:T(8,128)S(1)} %get-tuple-element.37), channel_id=1, source_target_pairs={{0,2},{1,0},{3,1},{2,3},{4,6},{5,4},{7,5},{6,7},{8,10},{9,8},{11,9... | collective-permute-start | bytes 196616 | tf_op jit(solution)/shard_map/ppermute | solution.py:45
  98.9 2.5 %collective-permute-done.32 = f32[128,128]{1,0:T(8,128)S(1)} collective-permute-done((f32[128,128]{1,0:T(8,128)S(1)}, f32[128,128]{1,0:T(8,128)S(1)}, u32[]{:S(2)}, u32[]{:S(2)}) %collective-permute-start.32) | collective-permute-done | bytes 65568 | tf_op jit(solution)/shard_map/ppermute | solution.py:45
  102.1 1.9 %collective-permute-start.35 = (f32[128,128]{1,0:T(8,128)S(1)}, f32[128,128]{1,0:T(8,128)S(1)}, u32[]{:S(2)}, u32[]{:S(2)}) collective-permute-start(f32[128,128]{1,0:T(8,128)S(1)} %collective-permute-done.31), channel_id=1, source_target_pairs={{0,2},{1,0},{3,1},{2,3},{4,6},{5,4},{7,5},{6,7},{8,10},{9,8},{11,9... | collective-permute-start | bytes 196616 | tf_op jit(solution)/shard_map/ppermute | solution.py:45
  104.3 2.1 %collective-permute-done.35 = f32[128,128]{1,0:T(8,128)S(1)} collective-permute-done((f32[128,128]{1,0:T(8,128)S(1)}, f32[128,128]{1,0:T(8,128)S(1)}, u32[]{:S(2)}, u32[]{:S(2)}) %collective-permute-start.35) | collective-permute-done | bytes 65568 | tf_op jit(solution)/shard_map/ppermute | solution.py:45
  107.5 2.8 %collective-permute-start.36 = (f32[128,128]{1,0:T(8,128)}, f32[128,128]{1,0:T(8,128)}, u32[]{:S(2)}, u32[]{:S(2)}) collective-permute-start(f32[128,128]{1,0:T(8,128)} %get-tuple-element.34), channel_id=1, source_target_pairs={{0,1},{1,3},{3,2},{2,0},{4,5},{5,7},{7,6},{6,4},{8,9},{9,11},{11,1... | collective-permute-start | bytes 196616 | tf_op jit(solution)/shard_map/ppermute | solution.py:45
  110.6 1.7 collective-permute-start.38
  112.3 1.2 collective-permute-start.37
  120.1 1.3 collective-permute-start.41
  122.6 2.1 %collective-permute-done.41 = f32[128,128]{1,0:T(8,128)S(1)} collective-permute-done((f32[128,128]{1,0:T(8,128)}, f32[128,128]{1,0:T(8,128)S(1)}, u32[]{:S(2)}, u32[]{:S(2)}) %collective-permute-start.41) | collective-permute-done | bytes 65568 | tf_op jit(solution)/shard_map/ppermute | solution.py:45
  125.1 1.9 %collective-permute-start.42 = (f32[128,128]{1,0:T(8,128)S(1)}, f32[128,128]{1,0:T(8,128)S(1)}, u32[]{:S(2)}, u32[]{:S(2)}) collective-permute-start(f32[128,128]{1,0:T(8,128)S(1)} %get-tuple-element.32), channel_id=1, source_target_pairs={{0,1},{1,3},{3,2},{2,0},{4,5},{5,7},{7,6},{6,4},{8,9},{9,11},{11,1... | collective-permute-start | bytes 196616 | tf_op jit(solution)/shard_map/ppermute | solution.py:45
  129.1 1.9 %collective-permute-start.43 = (f32[128,128]{1,0:T(8,128)S(1)}, f32[128,128]{1,0:T(8,128)S(1)}, u32[]{:S(2)}, u32[]{:S(2)}) collective-permute-start(f32[128,128]{1,0:T(8,128)S(1)} %get-tuple-element.33), channel_id=1, source_target_pairs={{0,2},{1,0},{3,1},{2,3},{4,6},{5,4},{7,5},{6,7},{8,10},{9,8},{11,9... | collective-permute-start | bytes 196616 | tf_op jit(solution)/shard_map/ppermute | solution.py:45
  131.9 1.4 collective-permute-done.44
  133.9 2.2 %collective-permute-start.47 = (f32[128,128]{1,0:T(8,128)S(1)}, f32[128,128]{1,0:T(8,128)S(1)}, u32[]{:S(2)}, u32[]{:S(2)}) collective-permute-start(f32[128,128]{1,0:T(8,128)S(1)} %collective-permute-done.43), channel_id=1, source_target_pairs={{0,2},{1,0},{3,1},{2,3},{4,6},{5,4},{7,5},{6,7},{8,10},{9,8},{11,9... | collective-permute-start | bytes 196616 | tf_op jit(solution)/shard_map/ppermute | solution.py:45
  136.5 1.8 collective-permute-done.47
  139.1 2.3 %collective-permute-start.49 = (f32[16,512]{1,0:T(8,128)S(1)}, f32[16,512]{1,0:T(8,128)S(1)}, u32[]{:S(2)}, u32[]{:S(2)}) collective-permute-start(f32[16,512]{1,0:T(8,128)S(1)} %get-tuple-element.28), channel_id=1, source_target_pairs={{0,8},{4,12},{8,16},{12,20},{16,24},{20,28},{24,0},{28,4},{1,9},{5... | collective-permute-start | bytes 98312 | tf_op jit(solution)/shard_map/ppermute | solution.py:94
  141.4 2.8 %collective-permute-start.50 = (f32[16,512]{1,0:T(8,128)S(1)}, f32[16,512]{1,0:T(8,128)S(1)}, u32[]{:S(2)}, u32[]{:S(2)}) collective-permute-start(f32[16,512]{1,0:T(8,128)S(1)} %get-tuple-element.27), channel_id=1, source_target_pairs={{0,12},{4,16},{8,20},{12,24},{16,28},{20,0},{24,4},{28,8},{1,13},{... | collective-permute-start | bytes 98312 | tf_op jit(solution)/shard_map/ppermute | solution.py:94
  144.9 1.5 collective-permute-start.53
  146.4 2.3 %collective-permute-start.54 = (f32[16,512]{1,0:T(8,128)S(1)}, f32[16,512]{1,0:T(8,128)S(1)}, u32[]{:S(2)}, u32[]{:S(2)}) collective-permute-start(f32[16,512]{1,0:T(8,128)S(1)} %get-tuple-element.23), channel_id=1, source_target_pairs={{0,28},{4,0},{8,4},{12,8},{16,12},{20,16},{24,20},{28,24},{1,29},{... | collective-permute-start | bytes 98312 | tf_op jit(solution)/shard_map/ppermute | solution.py:94
  148.9 1.4 collective-permute-done.54
  151.6 2.8 %collective-permute-start.55 = (f32[16,1280]{1,0:T(8,128)}, f32[16,1280]{1,0:T(8,128)S(1)}, u32[]{:S(2)}, u32[]{:S(2)}) collective-permute-start(f32[16,1280]{1,0:T(8,128)} %get-tuple-element.50), channel_id=1, source_target_pairs={{0,1},{1,2},{2,3},{3,0},{4,5},{5,6},{6,7},{7,4},{8,9},{9,10},{10,1... | collective-permute-start | bytes 245768 | tf_op jit(solution)/shard_map/ppermute | solution.py:94
  154.7 2.9 %collective-permute-start.57 = (f32[16,1280]{1,0:T(8,128)S(1)}, f32[16,1280]{1,0:T(8,128)}, u32[]{:S(2)}, u32[]{:S(2)}) collective-permute-start(f32[16,1280]{1,0:T(8,128)S(1)} %get-tuple-element.52), channel_id=1, source_target_pairs={{0,3},{1,0},{2,1},{3,2},{4,7},{5,4},{6,5},{7,6},{8,11},{9,8},{10,9... | collective-permute-start | bytes 245768 | tf_op jit(solution)/shard_map/ppermute | solution.py:94
  157.6 1.3 slice.173
  158.9 3.3 %collective-permute-done.56 = f32[16,1280]{1,0:T(8,128)S(1)} collective-permute-done((f32[16,1280]{1,0:T(8,128)S(1)}, f32[16,1280]{1,0:T(8,128)S(1)}, u32[]{:S(2)}, u32[]{:S(2)}) %collective-permute-start.56) | collective-permute-done | bytes 81952 | tf_op jit(solution)/shard_map/ppermute | solution.py:94
  163.1 1.7 fusion.37
  164.8 2.4 %collective-permute-start.58 = (f32[16,256]{1,0:T(8,128)S(1)}, f32[16,256]{1,0:T(8,128)S(1)}, u32[]{:S(2)}, u32[]{:S(2)}) collective-permute-start(f32[16,256]{1,0:T(8,128)S(1)} %fusion.37), channel_id=1, source_target_pairs={{0,1},{1,2},{2,3},{3,0},{4,5},{5,6},{6,7},{7,4},{8,9},{9,10},{10,1... | collective-permute-start | bytes 49160 | tf_op jit(solution)/shard_map/ppermute | solution.py:94
  167.3 1.6 collective-permute-start.60
  171.2 2.3 %collective-permute-done.59 = f32[16,256]{1,0:T(8,128)S(1)} collective-permute-done((f32[16,256]{1,0:T(8,128)S(1)}, f32[16,256]{1,0:T(8,128)S(1)}, u32[]{:S(2)}, u32[]{:S(2)}) %collective-permute-start.59) | collective-permute-done | bytes 16416 | tf_op jit(solution)/shard_map/ppermute | solution.py:94
  175.0 2.1 %collective-permute-start.62 = (f32[16,256]{1,0:T(8,128)S(1)}, f32[16,256]{1,0:T(8,128)S(1)}, u32[]{:S(2)}, u32[]{:S(2)}) collective-permute-start(f32[16,256]{1,0:T(8,128)S(1)} %slice_subtract_fusion), channel_id=1, source_target_pairs={{0,2},{1,3},{2,0},{3,1},{4,6},{5,7},{6,4},{7,5},{8,10},{9,11},{10,... | collective-permute-start | bytes 49160 | tf_op jit(solution)/shard_map/ppermute | solution.py:94
  177.1 1.3 collective-permute-start.63
  (218 shorter events, 50.1 us)
Async XLA Ops:
  2.3 21.0 %collective-permute-start = (f32[128,128]{1,0:T(8,128)}, f32[128,128]{1,0:T(8,128)}, u32[]{:S(2)}, u32[]{:S(2)}) collective-permute-start(f32[128,128]{1,0:T(8,128)} %get-tuple-element.21), channel_id=1, source_target_pairs={{0,1},{1,3},{3,2},{2,0},{4,5},{5,7},{7,6},{6,4},{8,9},{9,11},{11,1... | collective-permute-start | bytes 196616 | tf_op jit(solution)/shard_map/ppermute | solution.py:45
  5.3 20.8 %collective-permute-start.3 = (f32[128,128]{1,0:T(8,128)}, f32[128,128]{1,0:T(8,128)S(1)}, u32[]{:S(2)}, u32[]{:S(2)}) collective-permute-start(f32[128,128]{1,0:T(8,128)} %get-tuple-element.21), channel_id=1, source_target_pairs={{0,2},{1,0},{3,1},{2,3},{4,6},{5,4},{7,5},{6,7},{8,10},{9,8},{11,9... | collective-permute-start | bytes 196616 | tf_op jit(solution)/shard_map/ppermute | solution.py:45
  6.3 18.6 %collective-permute-start.2 = (f32[128,128]{1,0:T(8,128)}, f32[128,128]{1,0:T(8,128)S(1)}, u32[]{:S(2)}, u32[]{:S(2)}) collective-permute-start(f32[128,128]{1,0:T(8,128)} %get-tuple-element.22), channel_id=1, source_target_pairs={{0,1},{1,3},{3,2},{2,0},{4,5},{5,7},{7,6},{6,4},{8,9},{9,11},{11,1... | collective-permute-start | bytes 196616 | tf_op jit(solution)/shard_map/ppermute | solution.py:45
  7.9 13.8 %collective-permute-start.1 = (f32[128,128]{1,0:T(8,128)}, f32[128,128]{1,0:T(8,128)}, u32[]{:S(2)}, u32[]{:S(2)}) collective-permute-start(f32[128,128]{1,0:T(8,128)} %get-tuple-element.22), channel_id=1, source_target_pairs={{0,2},{1,0},{3,1},{2,3},{4,6},{5,4},{7,5},{6,7},{8,10},{9,8},{11,9... | collective-permute-start | bytes 196616 | tf_op jit(solution)/shard_map/ppermute | solution.py:45
  21.7 6.6 %collective-permute-start.5 = (f32[128,128]{1,0:T(8,128)}, f32[128,128]{1,0:T(8,128)S(1)}, u32[]{:S(2)}, u32[]{:S(2)}) collective-permute-start(f32[128,128]{1,0:T(8,128)} %collective-permute-done.1), channel_id=1, source_target_pairs={{0,2},{1,0},{3,1},{2,3},{4,6},{5,4},{7,5},{6,7},{8,10},{9,8},{11,9... | collective-permute-start | bytes 196616 | tf_op jit(solution)/shard_map/ppermute | solution.py:45
  23.3 6.2 %collective-permute-start.4 = (f32[128,128]{1,0:T(8,128)}, f32[128,128]{1,0:T(8,128)S(1)}, u32[]{:S(2)}, u32[]{:S(2)}) collective-permute-start(f32[128,128]{1,0:T(8,128)} %collective-permute-done), channel_id=1, source_target_pairs={{0,1},{1,3},{3,2},{2,0},{4,5},{5,7},{7,6},{6,4},{8,9},{9,11},{11,1... | collective-permute-start | bytes 196616 | tf_op jit(solution)/shard_map/ppermute | solution.py:45
  30.7 6.3 %collective-permute-start.6 = (f32[128,128]{1,0:T(8,128)S(1)}, f32[128,128]{1,0:T(8,128)S(1)}, u32[]{:S(2)}, u32[]{:S(2)}) collective-permute-start(f32[128,128]{1,0:T(8,128)S(1)} %get-tuple-element.44), channel_id=1, source_target_pairs={{0,1},{1,3},{3,2},{2,0},{4,5},{5,7},{7,6},{6,4},{8,9},{9,11},{11,1... | collective-permute-start | bytes 196616 | tf_op jit(solution)/shard_map/ppermute | solution.py:45
  33.3 7.6 %collective-permute-start.9 = (f32[128,128]{1,0:T(8,128)S(1)}, f32[128,128]{1,0:T(8,128)S(1)}, u32[]{:S(2)}, u32[]{:S(2)}) collective-permute-start(f32[128,128]{1,0:T(8,128)S(1)} %get-tuple-element.44), channel_id=1, source_target_pairs={{0,2},{1,0},{3,1},{2,3},{4,6},{5,4},{7,5},{6,7},{8,10},{9,8},{11,9... | collective-permute-start | bytes 196616 | tf_op jit(solution)/shard_map/ppermute | solution.py:45
  33.7 7.0 %collective-permute-start.8 = (f32[128,128]{1,0:T(8,128)S(1)}, f32[128,128]{1,0:T(8,128)S(1)}, u32[]{:S(2)}, u32[]{:S(2)}) collective-permute-start(f32[128,128]{1,0:T(8,128)S(1)} %get-tuple-element.45), channel_id=1, source_target_pairs={{0,1},{1,3},{3,2},{2,0},{4,5},{5,7},{7,6},{6,4},{8,9},{9,11},{11,1... | collective-permute-start | bytes 196616 | tf_op jit(solution)/shard_map/ppermute | solution.py:45
  35.3 5.9 %collective-permute-start.7 = (f32[128,128]{1,0:T(8,128)S(1)}, f32[128,128]{1,0:T(8,128)S(1)}, u32[]{:S(2)}, u32[]{:S(2)}) collective-permute-start(f32[128,128]{1,0:T(8,128)S(1)} %get-tuple-element.45), channel_id=1, source_target_pairs={{0,2},{1,0},{3,1},{2,3},{4,6},{5,4},{7,5},{6,7},{8,10},{9,8},{11,9... | collective-permute-start | bytes 196616 | tf_op jit(solution)/shard_map/ppermute | solution.py:45
  37.0 9.8 %collective-permute-start.10 = (f32[128,128]{1,0:T(8,128)S(1)}, f32[128,128]{1,0:T(8,128)S(1)}, u32[]{:S(2)}, u32[]{:S(2)}) collective-permute-start(f32[128,128]{1,0:T(8,128)S(1)} %collective-permute-done.6), channel_id=1, source_target_pairs={{0,1},{1,3},{3,2},{2,0},{4,5},{5,7},{7,6},{6,4},{8,9},{9,11},{11,1... | collective-permute-start | bytes 196616 | tf_op jit(solution)/shard_map/ppermute | solution.py:45
  41.2 5.3 %collective-permute-start.11 = (f32[128,128]{1,0:T(8,128)S(1)}, f32[128,128]{1,0:T(8,128)S(1)}, u32[]{:S(2)}, u32[]{:S(2)}) collective-permute-start(f32[128,128]{1,0:T(8,128)S(1)} %collective-permute-done.7), channel_id=1, source_target_pairs={{0,2},{1,0},{3,1},{2,3},{4,6},{5,4},{7,5},{6,7},{8,10},{9,8},{11,9... | collective-permute-start | bytes 196616 | tf_op jit(solution)/shard_map/ppermute | solution.py:45
  47.0 6.2 %collective-permute-start.12 = (f32[128,128]{1,0:T(8,128)S(1)}, f32[128,128]{1,0:T(8,128)S(1)}, u32[]{:S(2)}, u32[]{:S(2)}) collective-permute-start(f32[128,128]{1,0:T(8,128)S(1)} %get-tuple-element.42), channel_id=1, source_target_pairs={{0,1},{1,3},{3,2},{2,0},{4,5},{5,7},{7,6},{6,4},{8,9},{9,11},{11,1... | collective-permute-start | bytes 196616 | tf_op jit(solution)/shard_map/ppermute | solution.py:45
  49.3 6.1 %collective-permute-start.15 = (f32[128,128]{1,0:T(8,128)S(1)}, f32[128,128]{1,0:T(8,128)S(1)}, u32[]{:S(2)}, u32[]{:S(2)}) collective-permute-start(f32[128,128]{1,0:T(8,128)S(1)} %get-tuple-element.42), channel_id=1, source_target_pairs={{0,2},{1,0},{3,1},{2,3},{4,6},{5,4},{7,5},{6,7},{8,10},{9,8},{11,9... | collective-permute-start | bytes 196616 | tf_op jit(solution)/shard_map/ppermute | solution.py:45
  50.0 5.2 %collective-permute-start.14 = (f32[128,128]{1,0:T(8,128)S(1)}, f32[128,128]{1,0:T(8,128)S(1)}, u32[]{:S(2)}, u32[]{:S(2)}) collective-permute-start(f32[128,128]{1,0:T(8,128)S(1)} %get-tuple-element.43), channel_id=1, source_target_pairs={{0,1},{1,3},{3,2},{2,0},{4,5},{5,7},{7,6},{6,4},{8,9},{9,11},{11,1... | collective-permute-start | bytes 196616 | tf_op jit(solution)/shard_map/ppermute | solution.py:45
  51.3 4.5 %collective-permute-start.13 = (f32[128,128]{1,0:T(8,128)S(1)}, f32[128,128]{1,0:T(8,128)S(1)}, u32[]{:S(2)}, u32[]{:S(2)}) collective-permute-start(f32[128,128]{1,0:T(8,128)S(1)} %get-tuple-element.43), channel_id=1, source_target_pairs={{0,2},{1,0},{3,1},{2,3},{4,6},{5,4},{7,5},{6,7},{8,10},{9,8},{11,9... | collective-permute-start | bytes 196616 | tf_op jit(solution)/shard_map/ppermute | solution.py:45
  53.3 7.6 %collective-permute-start.16 = (f32[128,128]{1,0:T(8,128)S(1)}, f32[128,128]{1,0:T(8,128)S(1)}, u32[]{:S(2)}, u32[]{:S(2)}) collective-permute-start(f32[128,128]{1,0:T(8,128)S(1)} %collective-permute-done.12), channel_id=1, source_target_pairs={{0,1},{1,3},{3,2},{2,0},{4,5},{5,7},{7,6},{6,4},{8,9},{9,11},{11,1... | collective-permute-start | bytes 196616 | tf_op jit(solution)/shard_map/ppermute | solution.py:45
  55.9 4.7 %collective-permute-start.17 = (f32[128,128]{1,0:T(8,128)S(1)}, f32[128,128]{1,0:T(8,128)S(1)}, u32[]{:S(2)}, u32[]{:S(2)}) collective-permute-start(f32[128,128]{1,0:T(8,128)S(1)} %collective-permute-done.13), channel_id=1, source_target_pairs={{0,2},{1,0},{3,1},{2,3},{4,6},{5,4},{7,5},{6,7},{8,10},{9,8},{11,9... | collective-permute-start | bytes 196616 | tf_op jit(solution)/shard_map/ppermute | solution.py:45
  61.1 6.7 %collective-permute-start.18 = (f32[128,128]{1,0:T(8,128)S(1)}, f32[128,128]{1,0:T(8,128)S(1)}, u32[]{:S(2)}, u32[]{:S(2)}) collective-permute-start(f32[128,128]{1,0:T(8,128)S(1)} %get-tuple-element.40), channel_id=1, source_target_pairs={{0,1},{1,3},{3,2},{2,0},{4,5},{5,7},{7,6},{6,4},{8,9},{9,11},{11,1... | collective-permute-start | bytes 196616 | tf_op jit(solution)/shard_map/ppermute | solution.py:45
  64.0 6.2 %collective-permute-start.21 = (f32[128,128]{1,0:T(8,128)S(1)}, f32[128,128]{1,0:T(8,128)S(1)}, u32[]{:S(2)}, u32[]{:S(2)}) collective-permute-start(f32[128,128]{1,0:T(8,128)S(1)} %get-tuple-element.40), channel_id=1, source_target_pairs={{0,2},{1,0},{3,1},{2,3},{4,6},{5,4},{7,5},{6,7},{8,10},{9,8},{11,9... | collective-permute-start | bytes 196616 | tf_op jit(solution)/shard_map/ppermute | solution.py:45
  64.6 5.4 %collective-permute-start.20 = (f32[128,128]{1,0:T(8,128)S(1)}, f32[128,128]{1,0:T(8,128)S(1)}, u32[]{:S(2)}, u32[]{:S(2)}) collective-permute-start(f32[128,128]{1,0:T(8,128)S(1)} %get-tuple-element.41), channel_id=1, source_target_pairs={{0,1},{1,3},{3,2},{2,0},{4,5},{5,7},{7,6},{6,4},{8,9},{9,11},{11,1... | collective-permute-start | bytes 196616 | tf_op jit(solution)/shard_map/ppermute | solution.py:45
  66.0 4.6 %collective-permute-start.19 = (f32[128,128]{1,0:T(8,128)S(1)}, f32[128,128]{1,0:T(8,128)S(1)}, u32[]{:S(2)}, u32[]{:S(2)}) collective-permute-start(f32[128,128]{1,0:T(8,128)S(1)} %get-tuple-element.41), channel_id=1, source_target_pairs={{0,2},{1,0},{3,1},{2,3},{4,6},{5,4},{7,5},{6,7},{8,10},{9,8},{11,9... | collective-permute-start | bytes 196616 | tf_op jit(solution)/shard_map/ppermute | solution.py:45
  67.8 8.0 %collective-permute-start.22 = (f32[128,128]{1,0:T(8,128)S(1)}, f32[128,128]{1,0:T(8,128)S(1)}, u32[]{:S(2)}, u32[]{:S(2)}) collective-permute-start(f32[128,128]{1,0:T(8,128)S(1)} %collective-permute-done.18), channel_id=1, source_target_pairs={{0,1},{1,3},{3,2},{2,0},{4,5},{5,7},{7,6},{6,4},{8,9},{9,11},{11,1... | collective-permute-start | bytes 196616 | tf_op jit(solution)/shard_map/ppermute | solution.py:45
  70.7 4.9 %collective-permute-start.23 = (f32[128,128]{1,0:T(8,128)S(1)}, f32[128,128]{1,0:T(8,128)S(1)}, u32[]{:S(2)}, u32[]{:S(2)}) collective-permute-start(f32[128,128]{1,0:T(8,128)S(1)} %collective-permute-done.19), channel_id=1, source_target_pairs={{0,2},{1,0},{3,1},{2,3},{4,6},{5,4},{7,5},{6,7},{8,10},{9,8},{11,9... | collective-permute-start | bytes 196616 | tf_op jit(solution)/shard_map/ppermute | solution.py:45
  76.1 6.2 %collective-permute-start.24 = (f32[128,128]{1,0:T(8,128)S(1)}, f32[128,128]{1,0:T(8,128)S(1)}, u32[]{:S(2)}, u32[]{:S(2)}) collective-permute-start(f32[128,128]{1,0:T(8,128)S(1)} %get-tuple-element.38), channel_id=1, source_target_pairs={{0,1},{1,3},{3,2},{2,0},{4,5},{5,7},{7,6},{6,4},{8,9},{9,11},{11,1... | collective-permute-start | bytes 196616 | tf_op jit(solution)/shard_map/ppermute | solution.py:45
  78.4 6.7 %collective-permute-start.27 = (f32[128,128]{1,0:T(8,128)S(1)}, f32[128,128]{1,0:T(8,128)S(1)}, u32[]{:S(2)}, u32[]{:S(2)}) collective-permute-start(f32[128,128]{1,0:T(8,128)S(1)} %get-tuple-element.38), channel_id=1, source_target_pairs={{0,2},{1,0},{3,1},{2,3},{4,6},{5,4},{7,5},{6,7},{8,10},{9,8},{11,9... | collective-permute-start | bytes 196616 | tf_op jit(solution)/shard_map/ppermute | solution.py:45
  79.0 5.9 %collective-permute-start.26 = (f32[128,128]{1,0:T(8,128)S(1)}, f32[128,128]{1,0:T(8,128)S(1)}, u32[]{:S(2)}, u32[]{:S(2)}) collective-permute-start(f32[128,128]{1,0:T(8,128)S(1)} %get-tuple-element.39), channel_id=1, source_target_pairs={{0,1},{1,3},{3,2},{2,0},{4,5},{5,7},{7,6},{6,4},{8,9},{9,11},{11,1... | collective-permute-start | bytes 196616 | tf_op jit(solution)/shard_map/ppermute | solution.py:45
  80.4 6.4 %collective-permute-start.25 = (f32[128,128]{1,0:T(8,128)S(1)}, f32[128,128]{1,0:T(8,128)S(1)}, u32[]{:S(2)}, u32[]{:S(2)}) collective-permute-start(f32[128,128]{1,0:T(8,128)S(1)} %get-tuple-element.39), channel_id=1, source_target_pairs={{0,2},{1,0},{3,1},{2,3},{4,6},{5,4},{7,5},{6,7},{8,10},{9,8},{11,9... | collective-permute-start | bytes 196616 | tf_op jit(solution)/shard_map/ppermute | solution.py:45
  82.3 9.6 %collective-permute-start.28 = (f32[128,128]{1,0:T(8,128)S(1)}, f32[128,128]{1,0:T(8,128)S(1)}, u32[]{:S(2)}, u32[]{:S(2)}) collective-permute-start(f32[128,128]{1,0:T(8,128)S(1)} %collective-permute-done.24), channel_id=1, source_target_pairs={{0,1},{1,3},{3,2},{2,0},{4,5},{5,7},{7,6},{6,4},{8,9},{9,11},{11,1... | collective-permute-start | bytes 196616 | tf_op jit(solution)/shard_map/ppermute | solution.py:45
  86.8 4.9 %collective-permute-start.29 = (f32[128,128]{1,0:T(8,128)S(1)}, f32[128,128]{1,0:T(8,128)S(1)}, u32[]{:S(2)}, u32[]{:S(2)}) collective-permute-start(f32[128,128]{1,0:T(8,128)S(1)} %collective-permute-done.25), channel_id=1, source_target_pairs={{0,2},{1,0},{3,1},{2,3},{4,6},{5,4},{7,5},{6,7},{8,10},{9,8},{11,9... | collective-permute-start | bytes 196616 | tf_op jit(solution)/shard_map/ppermute | solution.py:45
  92.1 6.2 %collective-permute-start.30 = (f32[128,128]{1,0:T(8,128)S(1)}, f32[128,128]{1,0:T(8,128)S(1)}, u32[]{:S(2)}, u32[]{:S(2)}) collective-permute-start(f32[128,128]{1,0:T(8,128)S(1)} %get-tuple-element.36), channel_id=1, source_target_pairs={{0,1},{1,3},{3,2},{2,0},{4,5},{5,7},{7,6},{6,4},{8,9},{9,11},{11,1... | collective-permute-start | bytes 196616 | tf_op jit(solution)/shard_map/ppermute | solution.py:45
  93.8 7.9 %collective-permute-start.33 = (f32[128,128]{1,0:T(8,128)S(1)}, f32[128,128]{1,0:T(8,128)S(1)}, u32[]{:S(2)}, u32[]{:S(2)}) collective-permute-start(f32[128,128]{1,0:T(8,128)S(1)} %get-tuple-element.36), channel_id=1, source_target_pairs={{0,2},{1,0},{3,1},{2,3},{4,6},{5,4},{7,5},{6,7},{8,10},{9,8},{11,9... | collective-permute-start | bytes 196616 | tf_op jit(solution)/shard_map/ppermute | solution.py:45
  95.1 6.3 %collective-permute-start.32 = (f32[128,128]{1,0:T(8,128)S(1)}, f32[128,128]{1,0:T(8,128)S(1)}, u32[]{:S(2)}, u32[]{:S(2)}) collective-permute-start(f32[128,128]{1,0:T(8,128)S(1)} %get-tuple-element.37), channel_id=1, source_target_pairs={{0,1},{1,3},{3,2},{2,0},{4,5},{5,7},{7,6},{6,4},{8,9},{9,11},{11,1... | collective-permute-start | bytes 196616 | tf_op jit(solution)/shard_map/ppermute | solution.py:45
  95.8 6.3 %collective-permute-start.31 = (f32[128,128]{1,0:T(8,128)S(1)}, f32[128,128]{1,0:T(8,128)S(1)}, u32[]{:S(2)}, u32[]{:S(2)}) collective-permute-start(f32[128,128]{1,0:T(8,128)S(1)} %get-tuple-element.37), channel_id=1, source_target_pairs={{0,2},{1,0},{3,1},{2,3},{4,6},{5,4},{7,5},{6,7},{8,10},{9,8},{11,9... | collective-permute-start | bytes 196616 | tf_op jit(solution)/shard_map/ppermute | solution.py:45
  98.3 8.2 %collective-permute-start.34 = (f32[128,128]{1,0:T(8,128)S(1)}, f32[128,128]{1,0:T(8,128)S(1)}, u32[]{:S(2)}, u32[]{:S(2)}) collective-permute-start(f32[128,128]{1,0:T(8,128)S(1)} %collective-permute-done.30), channel_id=1, source_target_pairs={{0,1},{1,3},{3,2},{2,0},{4,5},{5,7},{7,6},{6,4},{8,9},{9,11},{11,1... | collective-permute-start | bytes 196616 | tf_op jit(solution)/shard_map/ppermute | solution.py:45
  102.1 4.3 %collective-permute-start.35 = (f32[128,128]{1,0:T(8,128)S(1)}, f32[128,128]{1,0:T(8,128)S(1)}, u32[]{:S(2)}, u32[]{:S(2)}) collective-permute-start(f32[128,128]{1,0:T(8,128)S(1)} %collective-permute-done.31), channel_id=1, source_target_pairs={{0,2},{1,0},{3,1},{2,3},{4,6},{5,4},{7,5},{6,7},{8,10},{9,8},{11,9... | collective-permute-start | bytes 196616 | tf_op jit(solution)/shard_map/ppermute | solution.py:45
  107.5 7.7 %collective-permute-start.36 = (f32[128,128]{1,0:T(8,128)}, f32[128,128]{1,0:T(8,128)}, u32[]{:S(2)}, u32[]{:S(2)}) collective-permute-start(f32[128,128]{1,0:T(8,128)} %get-tuple-element.34), channel_id=1, source_target_pairs={{0,1},{1,3},{3,2},{2,0},{4,5},{5,7},{7,6},{6,4},{8,9},{9,11},{11,1... | collective-permute-start | bytes 196616 | tf_op jit(solution)/shard_map/ppermute | solution.py:45
  110.3 8.8 %collective-permute-start.39 = (f32[128,128]{1,0:T(8,128)}, f32[128,128]{1,0:T(8,128)}, u32[]{:S(2)}, u32[]{:S(2)}) collective-permute-start(f32[128,128]{1,0:T(8,128)} %get-tuple-element.34), channel_id=1, source_target_pairs={{0,2},{1,0},{3,1},{2,3},{4,6},{5,4},{7,5},{6,7},{8,10},{9,8},{11,9... | collective-permute-start | bytes 196616 | tf_op jit(solution)/shard_map/ppermute | solution.py:45
  110.6 7.4 %collective-permute-start.38 = (f32[128,128]{1,0:T(8,128)}, f32[128,128]{1,0:T(8,128)}, u32[]{:S(2)}, u32[]{:S(2)}) collective-permute-start(f32[128,128]{1,0:T(8,128)} %get-tuple-element.35), channel_id=1, source_target_pairs={{0,1},{1,3},{3,2},{2,0},{4,5},{5,7},{7,6},{6,4},{8,9},{9,11},{11,1... | collective-permute-start | bytes 196616 | tf_op jit(solution)/shard_map/ppermute | solution.py:45
  112.3 7.8 %collective-permute-start.37 = (f32[128,128]{1,0:T(8,128)}, f32[128,128]{1,0:T(8,128)}, u32[]{:S(2)}, u32[]{:S(2)}) collective-permute-start(f32[128,128]{1,0:T(8,128)} %get-tuple-element.35), channel_id=1, source_target_pairs={{0,2},{1,0},{3,1},{2,3},{4,6},{5,4},{7,5},{6,7},{8,10},{9,8},{11,9... | collective-permute-start | bytes 196616 | tf_op jit(solution)/shard_map/ppermute | solution.py:45
  115.2 9.6 %collective-permute-start.40 = (f32[128,128]{1,0:T(8,128)}, f32[128,128]{1,0:T(8,128)S(1)}, u32[]{:S(2)}, u32[]{:S(2)}) collective-permute-start(f32[128,128]{1,0:T(8,128)} %collective-permute-done.36), channel_id=1, source_target_pairs={{0,1},{1,3},{3,2},{2,0},{4,5},{5,7},{7,6},{6,4},{8,9},{9,11},{11,1... | collective-permute-start | bytes 196616 | tf_op jit(solution)/shard_map/ppermute | solution.py:45
  120.1 4.5 %collective-permute-start.41 = (f32[128,128]{1,0:T(8,128)}, f32[128,128]{1,0:T(8,128)S(1)}, u32[]{:S(2)}, u32[]{:S(2)}) collective-permute-start(f32[128,128]{1,0:T(8,128)} %collective-permute-done.37), channel_id=1, source_target_pairs={{0,2},{1,0},{3,1},{2,3},{4,6},{5,4},{7,5},{6,7},{8,10},{9,8},{11,9... | collective-permute-start | bytes 196616 | tf_op jit(solution)/shard_map/ppermute | solution.py:45
  125.1 6.3 %collective-permute-start.42 = (f32[128,128]{1,0:T(8,128)S(1)}, f32[128,128]{1,0:T(8,128)S(1)}, u32[]{:S(2)}, u32[]{:S(2)}) collective-permute-start(f32[128,128]{1,0:T(8,128)S(1)} %get-tuple-element.32), channel_id=1, source_target_pairs={{0,1},{1,3},{3,2},{2,0},{4,5},{5,7},{7,6},{6,4},{8,9},{9,11},{11,1... | collective-permute-start | bytes 196616 | tf_op jit(solution)/shard_map/ppermute | solution.py:45
  127.0 6.6 %collective-permute-start.45 = (f32[128,128]{1,0:T(8,128)S(1)}, f32[128,128]{1,0:T(8,128)S(1)}, u32[]{:S(2)}, u32[]{:S(2)}) collective-permute-start(f32[128,128]{1,0:T(8,128)S(1)} %get-tuple-element.32), channel_id=1, source_target_pairs={{0,2},{1,0},{3,1},{2,3},{4,6},{5,4},{7,5},{6,7},{8,10},{9,8},{11,9... | collective-permute-start | bytes 196616 | tf_op jit(solution)/shard_map/ppermute | solution.py:45
  128.1 5.2 %collective-permute-start.44 = (f32[128,128]{1,0:T(8,128)S(1)}, f32[128,128]{1,0:T(8,128)S(1)}, u32[]{:S(2)}, u32[]{:S(2)}) collective-permute-start(f32[128,128]{1,0:T(8,128)S(1)} %get-tuple-element.33), channel_id=1, source_target_pairs={{0,1},{1,3},{3,2},{2,0},{4,5},{5,7},{7,6},{6,4},{8,9},{9,11},{11,1... | collective-permute-start | bytes 196616 | tf_op jit(solution)/shard_map/ppermute | solution.py:45
  129.1 4.9 %collective-permute-start.43 = (f32[128,128]{1,0:T(8,128)S(1)}, f32[128,128]{1,0:T(8,128)S(1)}, u32[]{:S(2)}, u32[]{:S(2)}) collective-permute-start(f32[128,128]{1,0:T(8,128)S(1)} %get-tuple-element.33), channel_id=1, source_target_pairs={{0,2},{1,0},{3,1},{2,3},{4,6},{5,4},{7,5},{6,7},{8,10},{9,8},{11,9... | collective-permute-start | bytes 196616 | tf_op jit(solution)/shard_map/ppermute | solution.py:45
  131.4 7.1 %collective-permute-start.46 = (f32[128,128]{1,0:T(8,128)S(1)}, f32[128,128]{1,0:T(8,128)S(1)}, u32[]{:S(2)}, u32[]{:S(2)}) collective-permute-start(f32[128,128]{1,0:T(8,128)S(1)} %collective-permute-done.42), channel_id=1, source_target_pairs={{0,1},{1,3},{3,2},{2,0},{4,5},{5,7},{7,6},{6,4},{8,9},{9,11},{11,1... | collective-permute-start | bytes 196616 | tf_op jit(solution)/shard_map/ppermute | solution.py:45
  133.9 4.3 %collective-permute-start.47 = (f32[128,128]{1,0:T(8,128)S(1)}, f32[128,128]{1,0:T(8,128)S(1)}, u32[]{:S(2)}, u32[]{:S(2)}) collective-permute-start(f32[128,128]{1,0:T(8,128)S(1)} %collective-permute-done.43), channel_id=1, source_target_pairs={{0,2},{1,0},{3,1},{2,3},{4,6},{5,4},{7,5},{6,7},{8,10},{9,8},{11,9... | collective-permute-start | bytes 196616 | tf_op jit(solution)/shard_map/ppermute | solution.py:45
  139.0 5.9 %collective-permute-start.48 = (f32[16,512]{1,0:T(8,128)S(1)}, f32[16,512]{1,0:T(8,128)S(1)}, u32[]{:S(2)}, u32[]{:S(2)}) collective-permute-start(f32[16,512]{1,0:T(8,128)S(1)} %get-tuple-element.29), channel_id=1, source_target_pairs={{0,4},{4,8},{8,12},{12,16},{16,20},{20,24},{24,28},{28,0},{1,5},{5... | collective-permute-start | bytes 98312 | tf_op jit(solution)/shard_map/ppermute | solution.py:94
  139.1 7.3 %collective-permute-start.49 = (f32[16,512]{1,0:T(8,128)S(1)}, f32[16,512]{1,0:T(8,128)S(1)}, u32[]{:S(2)}, u32[]{:S(2)}) collective-permute-start(f32[16,512]{1,0:T(8,128)S(1)} %get-tuple-element.28), channel_id=1, source_target_pairs={{0,8},{4,12},{8,16},{12,20},{16,24},{20,28},{24,0},{28,4},{1,9},{5... | collective-permute-start | bytes 98312 | tf_op jit(solution)/shard_map/ppermute | solution.py:94
  141.4 7.2 %collective-permute-start.50 = (f32[16,512]{1,0:T(8,128)S(1)}, f32[16,512]{1,0:T(8,128)S(1)}, u32[]{:S(2)}, u32[]{:S(2)}) collective-permute-start(f32[16,512]{1,0:T(8,128)S(1)} %get-tuple-element.27), channel_id=1, source_target_pairs={{0,12},{4,16},{8,20},{12,24},{16,28},{20,0},{24,4},{28,8},{1,13},{... | collective-permute-start | bytes 98312 | tf_op jit(solution)/shard_map/ppermute | solution.py:94
  144.2 4.4 %collective-permute-start.51 = (f32[16,512]{1,0:T(8,128)S(1)}, f32[16,512]{1,0:T(8,128)S(1)}, u32[]{:S(2)}, u32[]{:S(2)}) collective-permute-start(f32[16,512]{1,0:T(8,128)S(1)} %get-tuple-element.26), channel_id=1, source_target_pairs={{0,16},{4,20},{8,24},{12,28},{16,0},{20,4},{24,8},{28,12},{1,17},{... | collective-permute-start | bytes 98312 | tf_op jit(solution)/shard_map/ppermute | solution.py:94
  144.3 4.4 %collective-permute-start.52 = (f32[16,512]{1,0:T(8,128)S(1)}, f32[16,512]{1,0:T(8,128)S(1)}, u32[]{:S(2)}, u32[]{:S(2)}) collective-permute-start(f32[16,512]{1,0:T(8,128)S(1)} %get-tuple-element.25), channel_id=1, source_target_pairs={{0,20},{4,24},{8,28},{12,0},{16,4},{20,8},{24,12},{28,16},{1,21},{... | collective-permute-start | bytes 98312 | tf_op jit(solution)/shard_map/ppermute | solution.py:94
  144.9 4.0 %collective-permute-start.53 = (f32[16,512]{1,0:T(8,128)S(1)}, f32[16,512]{1,0:T(8,128)S(1)}, u32[]{:S(2)}, u32[]{:S(2)}) collective-permute-start(f32[16,512]{1,0:T(8,128)S(1)} %get-tuple-element.24), channel_id=1, source_target_pairs={{0,24},{4,28},{8,0},{12,4},{16,8},{20,12},{24,16},{28,20},{1,25},{... | collective-permute-start | bytes 98312 | tf_op jit(solution)/shard_map/ppermute | solution.py:94
  146.4 3.9 %collective-permute-start.54 = (f32[16,512]{1,0:T(8,128)S(1)}, f32[16,512]{1,0:T(8,128)S(1)}, u32[]{:S(2)}, u32[]{:S(2)}) collective-permute-start(f32[16,512]{1,0:T(8,128)S(1)} %get-tuple-element.23), channel_id=1, source_target_pairs={{0,28},{4,0},{8,4},{12,8},{16,12},{20,16},{24,20},{28,24},{1,29},{... | collective-permute-start | bytes 98312 | tf_op jit(solution)/shard_map/ppermute | solution.py:94
  151.6 7.3 %collective-permute-start.55 = (f32[16,1280]{1,0:T(8,128)}, f32[16,1280]{1,0:T(8,128)S(1)}, u32[]{:S(2)}, u32[]{:S(2)}) collective-permute-start(f32[16,1280]{1,0:T(8,128)} %get-tuple-element.50), channel_id=1, source_target_pairs={{0,1},{1,2},{2,3},{3,0},{4,5},{5,6},{6,7},{7,4},{8,9},{9,10},{10,1... | collective-permute-start | bytes 245768 | tf_op jit(solution)/shard_map/ppermute | solution.py:94
  154.4 7.8 %collective-permute-start.56 = (f32[16,1280]{1,0:T(8,128)S(1)}, f32[16,1280]{1,0:T(8,128)S(1)}, u32[]{:S(2)}, u32[]{:S(2)}) collective-permute-start(f32[16,1280]{1,0:T(8,128)S(1)} %get-tuple-element.51), channel_id=1, source_target_pairs={{0,2},{1,3},{2,0},{3,1},{4,6},{5,7},{6,4},{7,5},{8,10},{9,11},{10,... | collective-permute-start | bytes 245768 | tf_op jit(solution)/shard_map/ppermute | solution.py:94
  154.7 7.5 %collective-permute-start.57 = (f32[16,1280]{1,0:T(8,128)S(1)}, f32[16,1280]{1,0:T(8,128)}, u32[]{:S(2)}, u32[]{:S(2)}) collective-permute-start(f32[16,1280]{1,0:T(8,128)S(1)} %get-tuple-element.52), channel_id=1, source_target_pairs={{0,3},{1,0},{2,1},{3,2},{4,7},{5,4},{6,5},{7,6},{8,11},{9,8},{10,9... | collective-permute-start | bytes 245768 | tf_op jit(solution)/shard_map/ppermute | solution.py:94
  164.8 5.7 %collective-permute-start.58 = (f32[16,256]{1,0:T(8,128)S(1)}, f32[16,256]{1,0:T(8,128)S(1)}, u32[]{:S(2)}, u32[]{:S(2)}) collective-permute-start(f32[16,256]{1,0:T(8,128)S(1)} %fusion.37), channel_id=1, source_target_pairs={{0,1},{1,2},{2,3},{3,0},{4,5},{5,6},{6,7},{7,4},{8,9},{9,10},{10,1... | collective-permute-start | bytes 49160 | tf_op jit(solution)/shard_map/ppermute | solution.py:94
  167.3 3.7 %collective-permute-start.60 = (f32[16,256]{1,0:T(8,128)S(1)}, f32[16,256]{1,0:T(8,128)S(1)}, u32[]{:S(2)}, u32[]{:S(2)}) collective-permute-start(f32[16,256]{1,0:T(8,128)S(1)} %fusion.37), channel_id=1, source_target_pairs={{0,3},{1,0},{2,1},{3,2},{4,7},{5,4},{6,5},{7,6},{8,11},{9,8},{10,9... | collective-permute-start | bytes 49160 | tf_op jit(solution)/shard_map/ppermute | solution.py:94
  168.9 4.7 %collective-permute-start.59 = (f32[16,256]{1,0:T(8,128)S(1)}, f32[16,256]{1,0:T(8,128)S(1)}, u32[]{:S(2)}, u32[]{:S(2)}) collective-permute-start(f32[16,256]{1,0:T(8,128)S(1)} %fusion.37), channel_id=1, source_target_pairs={{0,2},{1,3},{2,0},{3,1},{4,6},{5,7},{6,4},{7,5},{8,10},{9,11},{10,... | collective-permute-start | bytes 49160 | tf_op jit(solution)/shard_map/ppermute | solution.py:94
  173.7 5.6 %collective-permute-start.61 = (f32[16,256]{1,0:T(8,128)S(1)}, f32[16,256]{1,0:T(8,128)S(1)}, u32[]{:S(2)}, u32[]{:S(2)}) collective-permute-start(f32[16,256]{1,0:T(8,128)S(1)} %slice_subtract_fusion), channel_id=1, source_target_pairs={{0,1},{1,2},{2,3},{3,0},{4,5},{5,6},{6,7},{7,4},{8,9},{9,10},{10,1... | collective-permute-start | bytes 49160 | tf_op jit(solution)/shard_map/ppermute | solution.py:94
  175.0 4.6 %collective-permute-start.62 = (f32[16,256]{1,0:T(8,128)S(1)}, f32[16,256]{1,0:T(8,128)S(1)}, u32[]{:S(2)}, u32[]{:S(2)}) collective-permute-start(f32[16,256]{1,0:T(8,128)S(1)} %slice_subtract_fusion), channel_id=1, source_target_pairs={{0,2},{1,3},{2,0},{3,1},{4,6},{5,7},{6,4},{7,5},{8,10},{9,11},{10,... | collective-permute-start | bytes 49160 | tf_op jit(solution)/shard_map/ppermute | solution.py:94
  177.1 3.7 %collective-permute-start.63 = (f32[16,256]{1,0:T(8,128)S(1)}, f32[16,256]{1,0:T(8,128)S(1)}, u32[]{:S(2)}, u32[]{:S(2)}) collective-permute-start(f32[16,256]{1,0:T(8,128)S(1)} %slice_subtract_fusion), channel_id=1, source_target_pairs={{0,3},{1,0},{2,1},{3,2},{4,7},{5,4},{6,5},{7,6},{8,11},{9,8},{10,9... | collective-permute-start | bytes 49160 | tf_op jit(solution)/shard_map/ppermute | solution.py:94
  (13 other events, 214.6 us)

commit v3 on v2

--- a/solution.py
+++ b/solution.py
@@ -54,37 +54,28 @@
 def ring_gather(value):
     members = lax.axis_size("grp")
     rows = value.shape[0]
-    half = rows // 2
-    low, high_part = value[:half], value[half:]
     pieces = [(lax.axis_index("grp") * rows, value)]
-    forward = [low, high_part]
-    backward = [low, high_part]
+    ahead = behind = value
     for distance in range(1, members // 2 + 1):
-        last = 2 * distance == members
-        ahead = ring_owner(distance) * rows
-        behind = ring_owner(-distance) * rows
-        if last:
-            forward[0] = ring_send(forward[0], 1)
-            backward[1] = ring_send(backward[1], -1)
-            pieces.append((ahead, forward[0]))
-            pieces.append((behind + half, backward[1]))
-        else:
-            forward[0] = ring_send(forward[0], 1)
-            backward[1] = ring_send(backward[1], -1)
-            forward[1] = ring_send(forward[1], 1)
-            backward[0] = ring_send(backward[0], -1)
-            pieces.append((ahead, forward[0]))
-            pieces.append((behind + half, backward[1]))
-            pieces.append((ahead + half, forward[1]))
-            pieces.append((behind, backward[0]))
+        ahead = ring_send(ahead, 1)
+        pieces.append((ring_owner(distance) * rows, ahead))
+        if 2 * distance < members:
+            behind = ring_send(behind, -1)
+            pieces.append((ring_owner(-distance) * rows, behind))
     return pieces
 
 
-def apply_rows(matrix, pieces):
+def columns_of(factor, index, offset, width):
+    lead = factor.ndim - 3
+    begin = (0,) * lead + (index, 0, offset)
+    size = (1,) * (lead + 1) + (factor.shape[-2], width)
+    return lax.dynamic_slice(factor, begin, size).reshape(factor.shape[-2], width)
+
+
+def apply_rows(factor, index, pieces):
     total = None
     for offset, piece in pieces:
-        columns = lax.dynamic_slice_in_dim(matrix, offset, piece.shape[0], 1)
-        term = product(columns, piece)
+        term = product(columns_of(factor, index, offset, piece.shape[0]), piece)
         total = term if total is None else total + term
     return total
 
@@ -94,7 +85,44 @@
     return lax.ppermute(value, axis, [(i, (i + shift) % count) for i in range(count)])
 
 
-def apply_wide(matrix, portion):
+def swap(value, axis, distance, block):
+    count = lax.axis_size(axis)
+    outer = count // block
+    if outer & (outer - 1):
+        pairs = [(i, (i // block + distance) % outer * block + i % block) for i in range(count)]
+    else:
+        pairs = [(i, (i // block ^ distance) * block + i % block) for i in range(count)]
+    return lax.ppermute(value, axis, pairs)
+
+
+def leaf_exchange(terms):
+    groups = lax.axis_size("leaf")
+    leaf = lax.axis_index("leaf")
+    inner = 2 if groups % 2 == 0 else 1
+    outer = groups // inner
+    width = terms.shape[1]
+    part = terms.shape[0] // groups
+    terms = terms.reshape(outer, inner, part, width)
+    inside = leaf % inner
+    held = [lax.dynamic_index_in_dim(terms, inside, 1, keepdims=False)]
+    if inner == 2:
+        away = lax.dynamic_index_in_dim(terms, 1 - inside, 1, keepdims=False)
+        pairs = [(i, i ^ 1) for i in range(groups)]
+        held.append(lax.ppermute(away, "leaf", pairs))
+    held = jnp.stack(held, axis=1)
+    outside = leaf // inner
+    parts = [lax.dynamic_index_in_dim(held, outside, 0, keepdims=False)]
+    for distance in range(1, outer):
+        if outer & (outer - 1):
+            target = lax.rem(outside + distance, outer)
+        else:
+            target = outside ^ distance
+        portion = lax.dynamic_index_in_dim(held, target, 0, keepdims=False)
+        parts.append(swap(portion, "leaf", distance, inner))
+    return jnp.concatenate(parts, axis=0)
+
+
+def apply_wide(factor, index, portion):
     members = lax.axis_size("grp")
     me = lax.axis_index("grp")
     rows = portion.shape[-1]
@@ -102,8 +130,7 @@
     for shift in range(members):
         piece = portion if shift == 0 else send(portion, "grp", shift)
         owner = lax.rem(me - shift + members, members)
-        columns = lax.dynamic_slice_in_dim(matrix, owner * rows, rows, 1)
-        term = contract_last(piece, columns)
+        term = contract_last(piece, columns_of(factor, index, owner * rows, rows))
         total = term if total is None else total + term
     return total
 
@@ -128,10 +155,8 @@
     sub_anc,
 ):
     rhs_group = rhs_local[0]
-    inverse_group = diag_inv_local[0]
-    below_group = sub_local[0]
     supernodes = rhs_group.shape[0]
-    order = inverse_group.shape[-1]
+    order = diag_inv_local.shape[-1]
     rhs_count = rhs_group.shape[-1]
     members = lax.axis_size("grp")
     groups = lax.axis_size("leaf")
@@ -151,11 +176,11 @@
     residual = rhs_group[0]
     chosen = jnp.zeros((slots, order, rhs_count), jnp.float32)
     for current in range(supernodes):
-        owned = apply_rows(inverse_group[current], ring_gather(residual))
+        owned = apply_rows(diag_inv_local, current, ring_gather(residual))
         solved.append(owned)
         pieces = ring_gather(owned)
         if current + 1 < supernodes:
-            residual = rhs_group[current + 1] - apply_rows(below_group[current], pieces)
+            residual = rhs_group[current + 1] - apply_rows(sub_local, current, pieces)
             whole = assemble(pieces, order)
             chosen = jnp.where((sources == current)[:, None, None], whole[None], chosen)
 
@@ -181,13 +206,7 @@
         [terms, jnp.broadcast_to(tag[None, :], (rhs_count, tile_rows))], axis=1
     )
 
-    received = [lax.dynamic_slice_in_dim(terms, leaf * part, part, 0)]
-    for shift in range(1, groups):
-        target = lax.rem(leaf + shift, groups)
-        received.append(
-            send(lax.dynamic_slice_in_dim(terms, target * part, part, 0), "leaf", shift)
-        )
-    received = jnp.stack(received)
+    received = leaf_exchange(terms)
     ancestors = rhs_anc.shape[0]
     block_count = ancestors * order // tile_rows
     width = slots * tile_rows
@@ -220,8 +239,8 @@
     solutions = [contract_last(total[:, :order], diag_inv_anc[0])]
     for ancestor in range(1, ancestors):
         begin = order + (ancestor - 1) * rows
-        residual = total[:, begin : begin + rows] - apply_wide(sub_anc[ancestor - 1], solutions[-1])
-        solutions.append(apply_wide(diag_inv_anc[ancestor], residual))
+        residual = total[:, begin : begin + rows] - apply_wide(sub_anc, ancestor - 1, solutions[-1])
+        solutions.append(apply_wide(diag_inv_anc, ancestor, residual))
     solutions = jnp.stack([jnp.transpose(s) for s in solutions])
     return (jnp.stack(solved)[None], solutions)
 

time: 183 us -> 182 us (level)
  starting transfers between devices: 91.8 us -> 42.8 us
  waiting for transfers between devices: 42.1 us -> 84.6 us
  other arithmetic: 4.3 us -> 11.1 us
  local copies, waits for them, and re-layouts: 13.9 us -> 11.2 us
  matrix products: 27.4 us -> 29.9 us
    ppermute x48 -> x24, starting transfers between devices: 67.8 us -> 28.9 us  [ring_send(): return lax.ppermute(value, 'grp', pairs)]
    ppermute x48 -> x24, waiting for transfers between devices: 31.6 us -> 68.2 us  [ring_send(): return lax.ppermute(value, 'grp', pairs)]
    ppermute x16 -> x9, starting transfers between devices: 24 us -> 10.4 us  [send(): lax.ppermute(value, axis, [(i, (i + shift) % count) for i in range(count)])]
    slice x11 -> x0, local copies, waits for them, and re-layouts: 11.7 us -> none  [the longest x1 4.4 us: on_device(): owned = apply_rows(inverse_group[current], ring_gather(residual))]
    ppermute x0 -> x4, waiting for transfers between devices: none -> 4.64 us  [the longest x3 2.95 us: swap(): return lax.ppermute(value, axis, pairs)]
    dot_general x49 -> x28, matrix products: 20.4 us -> 16.3 us  [product(): jnp.dot(left, right, precision=high, preferred_element_type=jnp.float32)]
    dot_general x9, matrix products: 3.31 us -> 7.11 us  [contract_last(): lax.dot_general(left, right, (((left.ndim - 1,), (right.ndim - 1,)), ((),...]
    ppermute x0 -> x4, starting transfers between devices: none -> 3.49 us  [the longest x3 3.49 us: swap(): return lax.ppermute(value, axis, pairs)]
  transfers between devices with their start and end apart: 64 -> 37, of which waited for: 29 -> 25; matrix products, arithmetic and copies ran while one was open for 19% -> 16% of each run, Pallas kernels for 0% -> 0%
where the time goes in v3:
time: 182 us; the launch traced here: 181 us
  waiting for transfers between devices  84.6 us (46%)
  starting transfers between devices  42.8 us (24%)
  matrix products  29.9 us (16%)
  local copies, waits for them, and re-layouts  11.2 us (6%)
  other arithmetic  11.1 us (6%)
  between operations  1.91 us (1%)
    ppermute x24, waiting for transfers between devices, ring_send(): return lax.ppermute(value, 'grp', pairs)  68.2 us
    ppermute x24, starting transfers between devices, ring_send(): return lax.ppermute(value, 'grp', pairs)  28.9 us
    dot_general x28, matrix products, product(): jnp.dot(left, right, precision=high, preferred_element_type=jnp.float32)  16.3 us
    ppermute x9, waiting for transfers between devices, send(): lax.ppermute(value, axis, [(i, (i + shift) % count) for i in range(count)])  11.7 us
    ppermute x9, starting transfers between devices, send(): lax.ppermute(value, axis, [(i, (i + shift) % count) for i in range(count)])  10.4 us
    dot_general x9, matrix products, contract_last(): lax.dot_general(left, right, (((left.ndim - 1,), (right.ndim - 1,)), ((),...  7.11 us
  transfers between devices with their start and end apart: 37, of which 25 were waited for; matrix products, arithmetic and copies ran while one was open for 16% of the time, Pallas kernels for 0%

profile of v3, /device:TPU:0, one launch (start us, length us, event | category | flops | bytes accessed | tf_op | source)
XLA Modules:
  0.0 181.4 jit_solution(1199703004304818172)
XLA Ops:
  0.6 1.1 slice_bitcast_fusion
  1.7 3.1 %collective-permute-start = (f32[256,128]{1,0:T(8,128)S(1)}, f32[256,128]{1,0:T(8,128)S(1)}, u32[]{:S(2)}, u32[]{:S(2)}) collective-permute-start(f32[256,128]{1,0:T(8,128)S(1)} %slice_bitcast_fusion), channel_id=1, source_target_pairs={{0,1},{1,3},{3,2},{2,0},{4,5},{5,7},{7,6},{6,4},{8,9},{9,11},{11,1... | collective-permute-start | bytes 393224 | tf_op jit(solution)/shard_map/ppermute | solution.py:45
  4.8 1.1 collective-permute-start.1
  7.8 1.3 fusion.74
  9.0 1.2 fusion.196
  11.1 1.8 %collective-permute-start.2 = (f32[256,128]{1,0:T(8,128)S(1)}, f32[256,128]{1,0:T(8,128)S(1)}, u32[]{:S(2)}, u32[]{:S(2)}) collective-permute-start(f32[256,128]{1,0:T(8,128)S(1)} %collective-permute-done), channel_id=1, source_target_pairs={{0,1},{1,3},{3,2},{2,0},{4,5},{5,7},{7,6},{6,4},{8,9},{9,11},{11,1... | collective-permute-start | bytes 393224 | tf_op jit(solution)/shard_map/ppermute | solution.py:45
  12.9 1.2 convolution_add_fusion.23
  14.2 1.3 convolution_add_fusion.22
  15.5 1.5 collective-permute-done.2
  17.0 1.2 constant_dynamic-update-slice_fusion.3
  18.3 2.3 %collective-permute-start.4 = (f32[256,128]{1,0:T(8,128)S(1)}, f32[256,128]{1,0:T(8,128)S(1)}, u32[]{:S(2)}, u32[]{:S(2)}) collective-permute-start(f32[256,128]{1,0:T(8,128)S(1)} %get-tuple-element.34), channel_id=1, source_target_pairs={{0,2},{1,0},{3,1},{2,3},{4,6},{5,4},{7,5},{6,7},{8,10},{9,8},{11,9... | collective-permute-start | bytes 393224 | tf_op jit(solution)/shard_map/ppermute | solution.py:45
  20.9 6.8 %collective-permute-done.3 = f32[256,128]{1,0:T(8,128)S(1)} collective-permute-done((f32[256,128]{1,0:T(8,128)S(1)}, f32[256,128]{1,0:T(8,128)S(1)}, u32[]{:S(2)}, u32[]{:S(2)}) %collective-permute-start.3) | collective-permute-done | bytes 131104 | tf_op jit(solution)/shard_map/ppermute | solution.py:45
  28.3 5.3 %collective-permute-done.5 = f32[256,128]{1,0:T(8,128)S(1)} collective-permute-done((f32[256,128]{1,0:T(8,128)S(1)}, f32[256,128]{1,0:T(8,128)S(1)}, u32[]{:S(2)}, u32[]{:S(2)}) %collective-permute-start.5) | collective-permute-done | bytes 131104 | tf_op jit(solution)/shard_map/ppermute | solution.py:45
  34.2 3.0 %collective-permute-start.7 = (f32[256,128]{1,0:T(8,128)S(1)}, f32[256,128]{1,0:T(8,128)S(1)}, u32[]{:S(2)}, u32[]{:S(2)}) collective-permute-start(f32[256,128]{1,0:T(8,128)S(1)} %fusion.8), channel_id=1, source_target_pairs={{0,2},{1,0},{3,1},{2,3},{4,6},{5,4},{7,5},{6,7},{8,10},{9,8},{11,9... | collective-permute-start | bytes 393224 | tf_op jit(solution)/shard_map/ppermute | solution.py:45
  37.2 2.7 %collective-permute-done.6 = f32[256,128]{1,0:T(8,128)S(1)} collective-permute-done((f32[256,128]{1,0:T(8,128)S(1)}, f32[256,128]{1,0:T(8,128)S(1)}, u32[]{:S(2)}, u32[]{:S(2)}) %collective-permute-start.6) | collective-permute-done | bytes 131104 | tf_op jit(solution)/shard_map/ppermute | solution.py:45
  41.5 5.6 %collective-permute-done.8 = f32[256,128]{1,0:T(8,128)S(1)} collective-permute-done((f32[256,128]{1,0:T(8,128)S(1)}, f32[256,128]{1,0:T(8,128)S(1)}, u32[]{:S(2)}, u32[]{:S(2)}) %collective-permute-start.8) | collective-permute-done | bytes 131104 | tf_op jit(solution)/shard_map/ppermute | solution.py:45
  48.0 1.5 collective-permute-start.9
  49.8 6.1 %collective-permute-done.9 = f32[256,128]{1,0:T(8,128)S(1)} collective-permute-done((f32[256,128]{1,0:T(8,128)S(1)}, f32[256,128]{1,0:T(8,128)S(1)}, u32[]{:S(2)}, u32[]{:S(2)}) %collective-permute-start.9) | collective-permute-done | bytes 131104 | tf_op jit(solution)/shard_map/ppermute | solution.py:45
  56.6 5.3 %collective-permute-done.11 = f32[256,128]{1,0:T(8,128)S(1)} collective-permute-done((f32[256,128]{1,0:T(8,128)S(1)}, f32[256,128]{1,0:T(8,128)S(1)}, u32[]{:S(2)}, u32[]{:S(2)}) %collective-permute-start.11) | collective-permute-done | bytes 131104 | tf_op jit(solution)/shard_map/ppermute | solution.py:45
  62.2 1.2 collective-permute-start.12
  63.7 1.8 %collective-permute-start.13 = (f32[256,128]{1,0:T(8,128)S(1)}, f32[256,128]{1,0:T(8,128)S(1)}, u32[]{:S(2)}, u32[]{:S(2)}) collective-permute-start(f32[256,128]{1,0:T(8,128)S(1)} %fusion.7), channel_id=1, source_target_pairs={{0,2},{1,0},{3,1},{2,3},{4,6},{5,4},{7,5},{6,7},{8,10},{9,8},{11,9... | collective-permute-start | bytes 393224 | tf_op jit(solution)/shard_map/ppermute | solution.py:45
  65.5 2.6 %collective-permute-done.12 = f32[256,128]{1,0:T(8,128)S(1)} collective-permute-done((f32[256,128]{1,0:T(8,128)S(1)}, f32[256,128]{1,0:T(8,128)S(1)}, u32[]{:S(2)}, u32[]{:S(2)}) %collective-permute-start.12) | collective-permute-done | bytes 131104 | tf_op jit(solution)/shard_map/ppermute | solution.py:45
  68.1 4.4 %collective-permute-start.14 = (f32[256,128]{1,0:T(8,128)S(1)}, f32[256,128]{1,0:T(8,128)S(1)}, u32[]{:S(2)}, u32[]{:S(2)}) collective-permute-start(f32[256,128]{1,0:T(8,128)S(1)} %collective-permute-done.12), channel_id=1, source_target_pairs={{0,1},{1,3},{3,2},{2,0},{4,5},{5,7},{7,6},{6,4},{8,9},{9,11},{11,1... | collective-permute-start | bytes 393224 | tf_op jit(solution)/shard_map/ppermute | solution.py:45
  73.1 3.6 %collective-permute-done.14 = f32[256,128]{1,0:T(8,128)S(1)} collective-permute-done((f32[256,128]{1,0:T(8,128)S(1)}, f32[256,128]{1,0:T(8,128)S(1)}, u32[]{:S(2)}, u32[]{:S(2)}) %collective-permute-start.14) | collective-permute-done | bytes 131104 | tf_op jit(solution)/shard_map/ppermute | solution.py:45
  77.0 2.4 %collective-permute-start.16 = (f32[256,128]{1,0:T(8,128)S(1)}, f32[256,128]{1,0:T(8,128)S(1)}, u32[]{:S(2)}, u32[]{:S(2)}) collective-permute-start(f32[256,128]{1,0:T(8,128)S(1)} %get-tuple-element.38), channel_id=1, source_target_pairs={{0,2},{1,0},{3,1},{2,3},{4,6},{5,4},{7,5},{6,7},{8,10},{9,8},{11,9... | collective-permute-start | bytes 393224 | tf_op jit(solution)/shard_map/ppermute | solution.py:45
  80.5 9.5 %collective-permute-done.15 = f32[256,128]{1,0:T(8,128)S(1)} collective-permute-done((f32[256,128]{1,0:T(8,128)S(1)}, f32[256,128]{1,0:T(8,128)S(1)}, u32[]{:S(2)}, u32[]{:S(2)}) %collective-permute-start.15) | collective-permute-done | bytes 131104 | tf_op jit(solution)/shard_map/ppermute | solution.py:45
  90.6 6.0 %collective-permute-done.17 = f32[256,128]{1,0:T(8,128)S(1)} collective-permute-done((f32[256,128]{1,0:T(8,128)S(1)}, f32[256,128]{1,0:T(8,128)S(1)}, u32[]{:S(2)}, u32[]{:S(2)}) %collective-permute-start.17) | collective-permute-done | bytes 131104 | tf_op jit(solution)/shard_map/ppermute | solution.py:45
  97.6 2.0 %collective-permute-start.18 = (f32[256,128]{1,0:T(8,128)}, f32[256,128]{1,0:T(8,128)}, u32[]{:S(2)}, u32[]{:S(2)}) collective-permute-start(f32[256,128]{1,0:T(8,128)} %fusion.6), channel_id=1, source_target_pairs={{0,1},{1,3},{3,2},{2,0},{4,5},{5,7},{7,6},{6,4},{8,9},{9,11},{11,1... | collective-permute-start | bytes 393224 | tf_op jit(solution)/shard_map/ppermute | solution.py:45
  99.6 1.9 %fusion = f32[3,128,128]{1,2,0:T(8,128)} fusion(f32[1,1,3,128,1024]{4,3,2,1,0:T(8,128)S(1)} %copy-done.1, f32[1024,128]{1,0:T(8,128)S(1)} %constant_dynamic-update-slice_fusion, f32[1024,128]{1,0:T(8,128)S(1)} %constant_dynamic-update-slice_fusion.4, f32[1024,128]{1,0:T(8,128)S(1)} %constant_dynamic-update-slice_fusion.8, ...), kind=kOutput, calls=%fused_computation | convolution fusion | flops 303169536 | bytes 3342345 | tf_op jit(solution)/shard_map/mtk,mkr->rmt/dot_general | solution.py:187
  101.5 1.7 copy.26
  103.3 1.4 fusion.49
  104.7 1.1 collective-permute-done.18
  106.0 1.3 convolution_add_fusion.5
  107.3 1.3 convolution_add_fusion.4
  108.6 3.5 %collective-permute-done.20 = f32[256,128]{1,0:T(8,128)S(1)} collective-permute-done((f32[256,128]{1,0:T(8,128)}, f32[256,128]{1,0:T(8,128)S(1)}, u32[]{:S(2)}, u32[]{:S(2)}) %collective-permute-start.20) | collective-permute-done | bytes 131104 | tf_op jit(solution)/shard_map/ppermute | solution.py:45
  112.1 1.2 convolution_add_fusion.3
  113.4 2.0 %collective-permute-start.21 = (f32[256,128]{1,0:T(8,128)S(1)}, f32[256,128]{1,0:T(8,128)S(1)}, u32[]{:S(2)}, u32[]{:S(2)}) collective-permute-start(f32[256,128]{1,0:T(8,128)S(1)} %convolution_add_fusion.3), channel_id=1, source_target_pairs={{0,1},{1,3},{3,2},{2,0},{4,5},{5,7},{7,6},{6,4},{8,9},{9,11},{11,1... | collective-permute-start | bytes 393224 | tf_op jit(solution)/shard_map/ppermute | solution.py:45
  115.4 1.4 fusion.26
  116.8 3.0 %collective-permute-done.21 = f32[256,128]{1,0:T(8,128)S(1)} collective-permute-done((f32[256,128]{1,0:T(8,128)S(1)}, f32[256,128]{1,0:T(8,128)S(1)}, u32[]{:S(2)}, u32[]{:S(2)}) %collective-permute-start.21) | collective-permute-done | bytes 131104 | tf_op jit(solution)/shard_map/ppermute | solution.py:45
  121.2 4.5 %collective-permute-done.23 = f32[256,128]{1,0:T(8,128)S(1)} collective-permute-done((f32[256,128]{1,0:T(8,128)S(1)}, f32[256,128]{1,0:T(8,128)S(1)}, u32[]{:S(2)}, u32[]{:S(2)}) %collective-permute-start.23) | collective-permute-done | bytes 131104 | tf_op jit(solution)/shard_map/ppermute | solution.py:45
  126.9 1.7 collective-permute-done.24
  128.6 1.6 fusion.119
  130.1 1.5 collective-permute-start.25
  131.6 1.5 collective-permute-start.26
  134.2 1.4 bitcast_dynamic-update-slice_fusion
  136.2 2.4 %collective-permute-done.27 = f32[2,16,512]{2,1,0:T(8,128)} collective-permute-done((f32[2,16,512]{2,1,0:T(8,128)}, f32[2,16,512]{2,1,0:T(8,128)}, u32[]{:S(2)}, u32[]{:S(2)}) %collective-permute-start.27) | collective-permute-done | bytes 65568 | tf_op jit(solution)/shard_map/ppermute | solution.py:95
  141.1 1.7 reshape.281
  142.8 1.9 %convolution_bitcast_fusion = f32[16,16,128]{2,1,0:T(8,128)} fusion(f32[8,16,3,128]{3,2,1,0:T(4,128)} %reshape.281, f32[8,3]{0,1:T(4,128)S(1)} %bitcast.243), kind=kOutput, calls=%fused_computation.9 | convolution fusion | flops 4718976 | bytes 327776 | tf_op jit(solution)/shard_map/gmq,grmt->rqt/dot_general | solution.py:217
  144.7 1.6 reshape.282
  148.7 2.4 %collective-permute-start.29 = (f32[16,1280]{1,0:T(8,128)}, f32[16,1280]{1,0:T(8,128)}, u32[]{:S(2)}, u32[]{:S(2)}) collective-permute-start(f32[16,1280]{1,0:T(8,128)} %get-tuple-element.27), channel_id=1, source_target_pairs={{0,2},{1,3},{2,0},{3,1},{4,6},{5,7},{6,4},{7,5},{8,10},{9,11},{10,... | collective-permute-start | bytes 245768 | tf_op jit(solution)/shard_map/ppermute | solution.py:85
  151.1 1.4 collective-permute-start.30
  152.5 3.0 %collective-permute-done.28 = f32[16,1280]{1,0:T(8,128)} collective-permute-done((f32[16,1280]{1,0:T(8,128)}, f32[16,1280]{1,0:T(8,128)}, u32[]{:S(2)}, u32[]{:S(2)}) %collective-permute-start.28) | collective-permute-done | bytes 81952 | tf_op jit(solution)/shard_map/ppermute | solution.py:85
  155.5 1.6 collective-permute-done.29
  158.1 1.7 fusion.13
  159.8 2.8 %collective-permute-start.33 = (f32[16,256]{1,0:T(8,128)S(1)}, f32[16,256]{1,0:T(8,128)S(1)}, u32[]{:S(2)}, u32[]{:S(2)}) collective-permute-start(f32[16,256]{1,0:T(8,128)S(1)} %fusion.13), channel_id=1, source_target_pairs={{0,3},{1,0},{2,1},{3,2},{4,7},{5,4},{6,5},{7,6},{8,11},{9,8},{10,9... | collective-permute-start | bytes 49160 | tf_op jit(solution)/shard_map/ppermute | solution.py:85
  163.3 1.1 fusion.38
  164.4 3.9 %collective-permute-done.31 = f32[16,256]{1,0:T(8,128)S(1)} collective-permute-done((f32[16,256]{1,0:T(8,128)S(1)}, f32[16,256]{1,0:T(8,128)S(1)}, u32[]{:S(2)}, u32[]{:S(2)}) %collective-permute-start.31) | collective-permute-done | bytes 16416 | tf_op jit(solution)/shard_map/ppermute | solution.py:85
  168.3 1.1 convolution_add_fusion.26
  169.5 1.1 fusion.34
  170.7 1.1 slice_subtract_fusion
  172.5 1.7 maximum_bitcast_fusion
  174.8 2.0 %collective-permute-start.34 = (f32[16,256]{1,0:T(8,128)S(1)}, f32[16,256]{1,0:T(8,128)S(1)}, u32[]{:S(2)}, u32[]{:S(2)}) collective-permute-start(f32[16,256]{1,0:T(8,128)S(1)} %slice_subtract_fusion), channel_id=1, source_target_pairs={{0,1},{1,2},{2,3},{3,0},{4,5},{5,6},{6,7},{7,4},{8,9},{9,10},{10,1... | collective-permute-start | bytes 49160 | tf_op jit(solution)/shard_map/ppermute | solution.py:85
  177.0 1.9 %collective-permute-done.35 = f32[16,256]{1,0:T(8,128)S(1)} collective-permute-done((f32[16,256]{1,0:T(8,128)S(1)}, f32[16,256]{1,0:T(8,128)S(1)}, u32[]{:S(2)}, u32[]{:S(2)}) %collective-permute-start.35) | collective-permute-done | bytes 16416 | tf_op jit(solution)/shard_map/ppermute | solution.py:85
  179.0 1.3 collective-permute-done.34
  (109 shorter events, 24.7 us)
Async XLA Ops:
  0.6 20.0 %copy-start = (f32[1,3,256,1024]{3,2,1,0:T(8,128)S(1)}, f32[1,3,256,1024]{3,2,1,0:T(8,128)}, u32[]{:S(2)}) copy-start(f32[1,3,256,1024]{3,2,1,0:T(8,128)} %param.14) | copy-start | bytes 9437188
  1.7 9.4 %collective-permute-start = (f32[256,128]{1,0:T(8,128)S(1)}, f32[256,128]{1,0:T(8,128)S(1)}, u32[]{:S(2)}, u32[]{:S(2)}) collective-permute-start(f32[256,128]{1,0:T(8,128)S(1)} %slice_bitcast_fusion), channel_id=1, source_target_pairs={{0,1},{1,3},{3,2},{2,0},{4,5},{5,7},{7,6},{6,4},{8,9},{9,11},{11,1... | collective-permute-start | bytes 393224 | tf_op jit(solution)/shard_map/ppermute | solution.py:45
  4.8 9.4 %collective-permute-start.1 = (f32[256,128]{1,0:T(8,128)S(1)}, f32[256,128]{1,0:T(8,128)}, u32[]{:S(2)}, u32[]{:S(2)}) collective-permute-start(f32[256,128]{1,0:T(8,128)S(1)} %slice_bitcast_fusion), channel_id=1, source_target_pairs={{0,2},{1,0},{3,1},{2,3},{4,6},{5,4},{7,5},{6,7},{8,10},{9,8},{11,9... | collective-permute-start | bytes 393224 | tf_op jit(solution)/shard_map/ppermute | solution.py:45
  10.3 23.3 %copy-start.6 = (f32[1,4,256,128]{3,2,1,0:T(8,128)S(1)}, f32[1,4,256,128]{3,2,1,0:T(8,128)}, u32[]{:S(2)}) copy-start(f32[1,4,256,128]{3,2,1,0:T(8,128)} %param.12) | copy-start | bytes 1572868
  10.3 23.7 %copy-start.3 = (f32[1,4,256,1024]{3,2,1,0:T(8,128)S(1)}, f32[1,4,256,1024]{3,2,1,0:T(8,128)}, u32[]{:S(2)}) copy-start(f32[1,4,256,1024]{3,2,1,0:T(8,128)} %param.13) | copy-start | bytes 12582916
  11.1 5.9 %collective-permute-start.2 = (f32[256,128]{1,0:T(8,128)S(1)}, f32[256,128]{1,0:T(8,128)S(1)}, u32[]{:S(2)}, u32[]{:S(2)}) collective-permute-start(f32[256,128]{1,0:T(8,128)S(1)} %collective-permute-done), channel_id=1, source_target_pairs={{0,1},{1,3},{3,2},{2,0},{4,5},{5,7},{7,6},{6,4},{8,9},{9,11},{11,1... | collective-permute-start | bytes 393224 | tf_op jit(solution)/shard_map/ppermute | solution.py:45
  18.3 9.7 %collective-permute-start.4 = (f32[256,128]{1,0:T(8,128)S(1)}, f32[256,128]{1,0:T(8,128)S(1)}, u32[]{:S(2)}, u32[]{:S(2)}) collective-permute-start(f32[256,128]{1,0:T(8,128)S(1)} %get-tuple-element.34), channel_id=1, source_target_pairs={{0,2},{1,0},{3,1},{2,3},{4,6},{5,4},{7,5},{6,7},{8,10},{9,8},{11,9... | collective-permute-start | bytes 393224 | tf_op jit(solution)/shard_map/ppermute | solution.py:45
  20.6 7.1 %collective-permute-start.3 = (f32[256,128]{1,0:T(8,128)S(1)}, f32[256,128]{1,0:T(8,128)S(1)}, u32[]{:S(2)}, u32[]{:S(2)}) collective-permute-start(f32[256,128]{1,0:T(8,128)S(1)} %get-tuple-element.34), channel_id=1, source_target_pairs={{0,1},{1,3},{3,2},{2,0},{4,5},{5,7},{7,6},{6,4},{8,9},{9,11},{11,1... | collective-permute-start | bytes 393224 | tf_op jit(solution)/shard_map/ppermute | solution.py:45
  27.7 5.9 %collective-permute-start.5 = (f32[256,128]{1,0:T(8,128)S(1)}, f32[256,128]{1,0:T(8,128)S(1)}, u32[]{:S(2)}, u32[]{:S(2)}) collective-permute-start(f32[256,128]{1,0:T(8,128)S(1)} %collective-permute-done.3), channel_id=1, source_target_pairs={{0,1},{1,3},{3,2},{2,0},{4,5},{5,7},{7,6},{6,4},{8,9},{9,11},{11,1... | collective-permute-start | bytes 393224 | tf_op jit(solution)/shard_map/ppermute | solution.py:45
  33.9 6.0 %collective-permute-start.6 = (f32[256,128]{1,0:T(8,128)S(1)}, f32[256,128]{1,0:T(8,128)S(1)}, u32[]{:S(2)}, u32[]{:S(2)}) collective-permute-start(f32[256,128]{1,0:T(8,128)S(1)} %fusion.8), channel_id=1, source_target_pairs={{0,1},{1,3},{3,2},{2,0},{4,5},{5,7},{7,6},{6,4},{8,9},{9,11},{11,1... | collective-permute-start | bytes 393224 | tf_op jit(solution)/shard_map/ppermute | solution.py:45
  34.2 7.0 %collective-permute-start.7 = (f32[256,128]{1,0:T(8,128)S(1)}, f32[256,128]{1,0:T(8,128)S(1)}, u32[]{:S(2)}, u32[]{:S(2)}) collective-permute-start(f32[256,128]{1,0:T(8,128)S(1)} %fusion.8), channel_id=1, source_target_pairs={{0,2},{1,0},{3,1},{2,3},{4,6},{5,4},{7,5},{6,7},{8,10},{9,8},{11,9... | collective-permute-start | bytes 393224 | tf_op jit(solution)/shard_map/ppermute | solution.py:45
  39.9 7.2 %collective-permute-start.8 = (f32[256,128]{1,0:T(8,128)S(1)}, f32[256,128]{1,0:T(8,128)S(1)}, u32[]{:S(2)}, u32[]{:S(2)}) collective-permute-start(f32[256,128]{1,0:T(8,128)S(1)} %collective-permute-done.6), channel_id=1, source_target_pairs={{0,1},{1,3},{3,2},{2,0},{4,5},{5,7},{7,6},{6,4},{8,9},{9,11},{11,1... | collective-permute-start | bytes 393224 | tf_op jit(solution)/shard_map/ppermute | solution.py:45
  47.5 8.8 %collective-permute-start.10 = (f32[256,128]{1,0:T(8,128)S(1)}, f32[256,128]{1,0:T(8,128)S(1)}, u32[]{:S(2)}, u32[]{:S(2)}) collective-permute-start(f32[256,128]{1,0:T(8,128)S(1)} %get-tuple-element.36), channel_id=1, source_target_pairs={{0,2},{1,0},{3,1},{2,3},{4,6},{5,4},{7,5},{6,7},{8,10},{9,8},{11,9... | collective-permute-start | bytes 393224 | tf_op jit(solution)/shard_map/ppermute | solution.py:45
  48.0 7.9 %collective-permute-start.9 = (f32[256,128]{1,0:T(8,128)S(1)}, f32[256,128]{1,0:T(8,128)S(1)}, u32[]{:S(2)}, u32[]{:S(2)}) collective-permute-start(f32[256,128]{1,0:T(8,128)S(1)} %get-tuple-element.36), channel_id=1, source_target_pairs={{0,1},{1,3},{3,2},{2,0},{4,5},{5,7},{7,6},{6,4},{8,9},{9,11},{11,1... | collective-permute-start | bytes 393224 | tf_op jit(solution)/shard_map/ppermute | solution.py:45
  56.0 6.0 %collective-permute-start.11 = (f32[256,128]{1,0:T(8,128)S(1)}, f32[256,128]{1,0:T(8,128)S(1)}, u32[]{:S(2)}, u32[]{:S(2)}) collective-permute-start(f32[256,128]{1,0:T(8,128)S(1)} %collective-permute-done.9), channel_id=1, source_target_pairs={{0,1},{1,3},{3,2},{2,0},{4,5},{5,7},{7,6},{6,4},{8,9},{9,11},{11,1... | collective-permute-start | bytes 393224 | tf_op jit(solution)/shard_map/ppermute | solution.py:45
  62.2 5.9 %collective-permute-start.12 = (f32[256,128]{1,0:T(8,128)S(1)}, f32[256,128]{1,0:T(8,128)S(1)}, u32[]{:S(2)}, u32[]{:S(2)}) collective-permute-start(f32[256,128]{1,0:T(8,128)S(1)} %fusion.7), channel_id=1, source_target_pairs={{0,1},{1,3},{3,2},{2,0},{4,5},{5,7},{7,6},{6,4},{8,9},{9,11},{11,1... | collective-permute-start | bytes 393224 | tf_op jit(solution)/shard_map/ppermute | solution.py:45
  63.7 35.9 %copy-start.1 = (f32[1,1,3,128,1024]{4,3,2,1,0:T(8,128)S(1)}, f32[1,1,3,128,1024]{4,3,2,1,0:T(8,128)}, u32[]{:S(2)}) copy-start(f32[1,1,3,128,1024]{4,3,2,1,0:T(8,128)} %param.15) | copy-start | bytes 4718596
  63.7 9.1 %collective-permute-start.13 = (f32[256,128]{1,0:T(8,128)S(1)}, f32[256,128]{1,0:T(8,128)S(1)}, u32[]{:S(2)}, u32[]{:S(2)}) collective-permute-start(f32[256,128]{1,0:T(8,128)S(1)} %fusion.7), channel_id=1, source_target_pairs={{0,2},{1,0},{3,1},{2,3},{4,6},{5,4},{7,5},{6,7},{8,10},{9,8},{11,9... | collective-permute-start | bytes 393224 | tf_op jit(solution)/shard_map/ppermute | solution.py:45
  68.1 8.5 %collective-permute-start.14 = (f32[256,128]{1,0:T(8,128)S(1)}, f32[256,128]{1,0:T(8,128)S(1)}, u32[]{:S(2)}, u32[]{:S(2)}) collective-permute-start(f32[256,128]{1,0:T(8,128)S(1)} %collective-permute-done.12), channel_id=1, source_target_pairs={{0,1},{1,3},{3,2},{2,0},{4,5},{5,7},{7,6},{6,4},{8,9},{9,11},{11,1... | collective-permute-start | bytes 393224 | tf_op jit(solution)/shard_map/ppermute | solution.py:45
  77.0 13.3 %collective-permute-start.16 = (f32[256,128]{1,0:T(8,128)S(1)}, f32[256,128]{1,0:T(8,128)S(1)}, u32[]{:S(2)}, u32[]{:S(2)}) collective-permute-start(f32[256,128]{1,0:T(8,128)S(1)} %get-tuple-element.38), channel_id=1, source_target_pairs={{0,2},{1,0},{3,1},{2,3},{4,6},{5,4},{7,5},{6,7},{8,10},{9,8},{11,9... | collective-permute-start | bytes 393224 | tf_op jit(solution)/shard_map/ppermute | solution.py:45
  79.4 10.6 %collective-permute-start.15 = (f32[256,128]{1,0:T(8,128)S(1)}, f32[256,128]{1,0:T(8,128)S(1)}, u32[]{:S(2)}, u32[]{:S(2)}) collective-permute-start(f32[256,128]{1,0:T(8,128)S(1)} %get-tuple-element.38), channel_id=1, source_target_pairs={{0,1},{1,3},{3,2},{2,0},{4,5},{5,7},{7,6},{6,4},{8,9},{9,11},{11,1... | collective-permute-start | bytes 393224 | tf_op jit(solution)/shard_map/ppermute | solution.py:45
  90.0 6.6 %collective-permute-start.17 = (f32[256,128]{1,0:T(8,128)S(1)}, f32[256,128]{1,0:T(8,128)S(1)}, u32[]{:S(2)}, u32[]{:S(2)}) collective-permute-start(f32[256,128]{1,0:T(8,128)S(1)} %collective-permute-done.15), channel_id=1, source_target_pairs={{0,1},{1,3},{3,2},{2,0},{4,5},{5,7},{7,6},{6,4},{8,9},{9,11},{11,1... | collective-permute-start | bytes 393224 | tf_op jit(solution)/shard_map/ppermute | solution.py:45
  97.6 9.8 %collective-permute-start.19 = (f32[256,128]{1,0:T(8,128)}, f32[256,128]{1,0:T(8,128)}, u32[]{:S(2)}, u32[]{:S(2)}) collective-permute-start(f32[256,128]{1,0:T(8,128)} %fusion.6), channel_id=1, source_target_pairs={{0,2},{1,0},{3,1},{2,3},{4,6},{5,4},{7,5},{6,7},{8,10},{9,8},{11,9... | collective-permute-start | bytes 393224 | tf_op jit(solution)/shard_map/ppermute | solution.py:45
  97.6 8.2 %collective-permute-start.18 = (f32[256,128]{1,0:T(8,128)}, f32[256,128]{1,0:T(8,128)}, u32[]{:S(2)}, u32[]{:S(2)}) collective-permute-start(f32[256,128]{1,0:T(8,128)} %fusion.6), channel_id=1, source_target_pairs={{0,1},{1,3},{3,2},{2,0},{4,5},{5,7},{7,6},{6,4},{8,9},{9,11},{11,1... | collective-permute-start | bytes 393224 | tf_op jit(solution)/shard_map/ppermute | solution.py:45
  101.5 24.2 %copy-start.9 = (pred[384]{0:T(512)(128)(4,1)S(1)}, pred[384]{0:T(512)(128)(4,1)}, u32[]{:S(2)}) copy-start(pred[384]{0:T(512)(128)(4,1)} %broadcast_bitcast_fusion) | copy-start | bytes 1156
  103.3 17.1 %copy-start.2 = (f32[1,1,3,128,1024]{4,3,2,1,0:T(8,128)S(1)}, f32[1,1,3,128,1024]{4,3,2,1,0:T(8,128)}, u32[]{:S(2)}) copy-start(f32[1,1,3,128,1024]{4,3,2,1,0:T(8,128)} %param.15) | copy-start | bytes 4718596
  103.3 22.4 %copy-start.7 = (f32[128,384]{1,0:T(8,128)S(1)}, f32[128,384]{1,0:T(8,128)}, u32[]{:S(2)}) copy-start(f32[128,384]{1,0:T(8,128)} %copy.26) | copy-start | bytes 589828
  105.8 6.3 %collective-permute-start.20 = (f32[256,128]{1,0:T(8,128)}, f32[256,128]{1,0:T(8,128)S(1)}, u32[]{:S(2)}, u32[]{:S(2)}) collective-permute-start(f32[256,128]{1,0:T(8,128)} %collective-permute-done.18), channel_id=1, source_target_pairs={{0,1},{1,3},{3,2},{2,0},{4,5},{5,7},{7,6},{6,4},{8,9},{9,11},{11,1... | collective-permute-start | bytes 393224 | tf_op jit(solution)/shard_map/ppermute | solution.py:45
  113.3 2.1 %copy-start.5 = (f32[256,128]{1,0:T(8,128)}, f32[256,128]{1,0:T(8,128)S(1)}, u32[]{:S(2)}) copy-start(f32[256,128]{1,0:T(8,128)S(1)} %convolution_add_fusion.3) | copy-start | bytes 393220
  113.3 7.5 %collective-permute-start.22 = (f32[256,128]{1,0:T(8,128)S(1)}, f32[256,128]{1,0:T(8,128)S(1)}, u32[]{:S(2)}, u32[]{:S(2)}) collective-permute-start(f32[256,128]{1,0:T(8,128)S(1)} %convolution_add_fusion.3), channel_id=1, source_target_pairs={{0,2},{1,0},{3,1},{2,3},{4,6},{5,4},{7,5},{6,7},{8,10},{9,8},{11,9... | collective-permute-start | bytes 393224 | tf_op jit(solution)/shard_map/ppermute | solution.py:45
  113.4 6.4 %collective-permute-start.21 = (f32[256,128]{1,0:T(8,128)S(1)}, f32[256,128]{1,0:T(8,128)S(1)}, u32[]{:S(2)}, u32[]{:S(2)}) collective-permute-start(f32[256,128]{1,0:T(8,128)S(1)} %convolution_add_fusion.3), channel_id=1, source_target_pairs={{0,1},{1,3},{3,2},{2,0},{4,5},{5,7},{7,6},{6,4},{8,9},{9,11},{11,1... | collective-permute-start | bytes 393224 | tf_op jit(solution)/shard_map/ppermute | solution.py:45
  119.8 5.9 %collective-permute-start.23 = (f32[256,128]{1,0:T(8,128)S(1)}, f32[256,128]{1,0:T(8,128)S(1)}, u32[]{:S(2)}, u32[]{:S(2)}) collective-permute-start(f32[256,128]{1,0:T(8,128)S(1)} %collective-permute-done.21), channel_id=1, source_target_pairs={{0,1},{1,3},{3,2},{2,0},{4,5},{5,7},{7,6},{6,4},{8,9},{9,11},{11,1... | collective-permute-start | bytes 393224 | tf_op jit(solution)/shard_map/ppermute | solution.py:45
  126.9 1.7 collective-permute-start.24
  130.1 5.5 %collective-permute-start.25 = (f32[2,16,512]{2,1,0:T(8,128)}, f32[2,16,512]{2,1,0:T(8,128)}, u32[]{:S(2)}, u32[]{:S(2)}) collective-permute-start(f32[2,16,512]{2,1,0:T(8,128)} %get-tuple-element.15), channel_id=1, source_target_pairs={{0,8},{4,12},{8,0},{12,4},{16,24},{20,28},{24,16},{28,20},{1,9},{5... | collective-permute-start | bytes 196616 | tf_op jit(solution)/shard_map/ppermute | solution.py:95
  131.6 4.6 %collective-permute-start.26 = (f32[2,16,512]{2,1,0:T(8,128)}, f32[2,16,512]{2,1,0:T(8,128)}, u32[]{:S(2)}, u32[]{:S(2)}) collective-permute-start(f32[2,16,512]{2,1,0:T(8,128)} %get-tuple-element.16), channel_id=1, source_target_pairs={{0,16},{4,20},{8,24},{12,28},{16,0},{20,4},{24,8},{28,12},{1,17},{... | collective-permute-start | bytes 196616 | tf_op jit(solution)/shard_map/ppermute | solution.py:95
  133.1 5.5 %collective-permute-start.27 = (f32[2,16,512]{2,1,0:T(8,128)}, f32[2,16,512]{2,1,0:T(8,128)}, u32[]{:S(2)}, u32[]{:S(2)}) collective-permute-start(f32[2,16,512]{2,1,0:T(8,128)} %get-tuple-element.17), channel_id=1, source_target_pairs={{0,24},{4,28},{8,16},{12,20},{16,8},{20,12},{24,0},{28,4},{1,25},{... | collective-permute-start | bytes 196616 | tf_op jit(solution)/shard_map/ppermute | solution.py:95
  147.4 0.6 copy-start.8
  148.7 6.8 %collective-permute-start.28 = (f32[16,1280]{1,0:T(8,128)}, f32[16,1280]{1,0:T(8,128)}, u32[]{:S(2)}, u32[]{:S(2)}) collective-permute-start(f32[16,1280]{1,0:T(8,128)} %get-tuple-element.26), channel_id=1, source_target_pairs={{0,1},{1,2},{2,3},{3,0},{4,5},{5,6},{6,7},{7,4},{8,9},{9,10},{10,1... | collective-permute-start | bytes 245768 | tf_op jit(solution)/shard_map/ppermute | solution.py:85
  148.7 8.4 %collective-permute-start.29 = (f32[16,1280]{1,0:T(8,128)}, f32[16,1280]{1,0:T(8,128)}, u32[]{:S(2)}, u32[]{:S(2)}) collective-permute-start(f32[16,1280]{1,0:T(8,128)} %get-tuple-element.27), channel_id=1, source_target_pairs={{0,2},{1,3},{2,0},{3,1},{4,6},{5,7},{6,4},{7,5},{8,10},{9,11},{10,... | collective-permute-start | bytes 245768 | tf_op jit(solution)/shard_map/ppermute | solution.py:85
  151.1 6.0 %collective-permute-start.30 = (f32[16,1280]{1,0:T(8,128)}, f32[16,1280]{1,0:T(8,128)}, u32[]{:S(2)}, u32[]{:S(2)}) collective-permute-start(f32[16,1280]{1,0:T(8,128)} %get-tuple-element.28), channel_id=1, source_target_pairs={{0,3},{1,0},{2,1},{3,2},{4,7},{5,4},{6,5},{7,6},{8,11},{9,8},{10,9... | collective-permute-start | bytes 245768 | tf_op jit(solution)/shard_map/ppermute | solution.py:85
  152.5 24.3 %copy-start.4 = (f32[2,256,1024]{2,1,0:T(8,128)S(1)}, f32[2,256,1024]{2,1,0:T(8,128)}, u32[]{:S(2)}) copy-start(f32[2,256,1024]{2,1,0:T(8,128)} %param.20) | copy-start | bytes 6291460
  159.8 9.7 %collective-permute-start.33 = (f32[16,256]{1,0:T(8,128)S(1)}, f32[16,256]{1,0:T(8,128)S(1)}, u32[]{:S(2)}, u32[]{:S(2)}) collective-permute-start(f32[16,256]{1,0:T(8,128)S(1)} %fusion.13), channel_id=1, source_target_pairs={{0,3},{1,0},{2,1},{3,2},{4,7},{5,4},{6,5},{7,6},{8,11},{9,8},{10,9... | collective-permute-start | bytes 49160 | tf_op jit(solution)/shard_map/ppermute | solution.py:85
  162.7 8.0 %collective-permute-start.32 = (f32[16,256]{1,0:T(8,128)S(1)}, f32[16,256]{1,0:T(8,128)S(1)}, u32[]{:S(2)}, u32[]{:S(2)}) collective-permute-start(f32[16,256]{1,0:T(8,128)S(1)} %fusion.13), channel_id=1, source_target_pairs={{0,2},{1,3},{2,0},{3,1},{4,6},{5,7},{6,4},{7,5},{8,10},{9,11},{10,... | collective-permute-start | bytes 49160 | tf_op jit(solution)/shard_map/ppermute | solution.py:85
  162.8 5.5 %collective-permute-start.31 = (f32[16,256]{1,0:T(8,128)S(1)}, f32[16,256]{1,0:T(8,128)S(1)}, u32[]{:S(2)}, u32[]{:S(2)}) collective-permute-start(f32[16,256]{1,0:T(8,128)S(1)} %fusion.13), channel_id=1, source_target_pairs={{0,1},{1,2},{2,3},{3,0},{4,5},{5,6},{6,7},{7,4},{8,9},{9,10},{10,1... | collective-permute-start | bytes 49160 | tf_op jit(solution)/shard_map/ppermute | solution.py:85
  171.9 4.8 %collective-permute-start.36 = (f32[16,256]{1,0:T(8,128)S(1)}, f32[16,256]{1,0:T(8,128)S(1)}, u32[]{:S(2)}, u32[]{:S(2)}) collective-permute-start(f32[16,256]{1,0:T(8,128)S(1)} %slice_subtract_fusion), channel_id=1, source_target_pairs={{0,3},{1,0},{2,1},{3,2},{4,7},{5,4},{6,5},{7,6},{8,11},{9,8},{10,9... | collective-permute-start | bytes 49160 | tf_op jit(solution)/shard_map/ppermute | solution.py:85
  174.2 4.6 %collective-permute-start.35 = (f32[16,256]{1,0:T(8,128)S(1)}, f32[16,256]{1,0:T(8,128)S(1)}, u32[]{:S(2)}, u32[]{:S(2)}) collective-permute-start(f32[16,256]{1,0:T(8,128)S(1)} %slice_subtract_fusion), channel_id=1, source_target_pairs={{0,2},{1,3},{2,0},{3,1},{4,6},{5,7},{6,4},{7,5},{8,10},{9,11},{10,... | collective-permute-start | bytes 49160 | tf_op jit(solution)/shard_map/ppermute | solution.py:85
  174.8 5.5 %collective-permute-start.34 = (f32[16,256]{1,0:T(8,128)S(1)}, f32[16,256]{1,0:T(8,128)S(1)}, u32[]{:S(2)}, u32[]{:S(2)}) collective-permute-start(f32[16,256]{1,0:T(8,128)S(1)} %slice_subtract_fusion), channel_id=1, source_target_pairs={{0,1},{1,2},{2,3},{3,0},{4,5},{5,6},{6,7},{7,4},{8,9},{9,10},{10,1... | collective-permute-start | bytes 49160 | tf_op jit(solution)/shard_map/ppermute | solution.py:85

commit v4 on v3

--- a/solution.py
+++ b/solution.py
@@ -20,48 +20,19 @@
     )
 
 
-def ring_member(place, members):
-    if place == 0:
-        return 0
-    return 2 * place - 1 if place <= members // 2 else 2 * (members - place)
-
-
-def ring_place_of(member, members):
-    return jnp.where(
-        member % 2 == 1, (member + 1) // 2, jnp.where(member == 0, 0, members - member // 2)
-    )
-
-
-def ring_member_of(place, members):
-    return jnp.where(place <= members // 2, jnp.maximum(2 * place - 1, 0), 2 * (members - place))
-
-
-def ring_send(value, step):
+def send(value, axis, shift):
+    count = lax.axis_size(axis)
+    return lax.ppermute(value, axis, [(i, (i + shift) % count) for i in range(count)])
+
+
+def gather_rows(value):
     members = lax.axis_size("grp")
-    pairs = [
-        (ring_member(p, members), ring_member((p + step) % members, members))
-        for p in range(members)
-    ]
-    return lax.ppermute(value, "grp", pairs)
-
-
-def ring_owner(distance):
-    members = lax.axis_size("grp")
-    place = ring_place_of(lax.axis_index("grp"), members)
-    return ring_member_of(lax.rem(place - distance + members, members), members)
-
-
-def ring_gather(value):
-    members = lax.axis_size("grp")
+    me = lax.axis_index("grp")
     rows = value.shape[0]
-    pieces = [(lax.axis_index("grp") * rows, value)]
-    ahead = behind = value
-    for distance in range(1, members // 2 + 1):
-        ahead = ring_send(ahead, 1)
-        pieces.append((ring_owner(distance) * rows, ahead))
-        if 2 * distance < members:
-            behind = ring_send(behind, -1)
-            pieces.append((ring_owner(-distance) * rows, behind))
+    pieces = [(me * rows, value)]
+    for shift in range(1, members):
+        owner = lax.rem(me - shift + members, members)
+        pieces.append((owner * rows, send(value, "grp", shift)))
     return pieces
 
 
@@ -78,11 +49,6 @@
         term = product(columns_of(factor, index, offset, piece.shape[0]), piece)
         total = term if total is None else total + term
     return total
-
-
-def send(value, axis, shift):
-    count = lax.axis_size(axis)
-    return lax.ppermute(value, axis, [(i, (i + shift) % count) for i in range(count)])
 
 
 def swap(value, axis, distance, block):
@@ -176,9 +142,9 @@
     residual = rhs_group[0]
     chosen = jnp.zeros((slots, order, rhs_count), jnp.float32)
     for current in range(supernodes):
-        owned = apply_rows(diag_inv_local, current, ring_gather(residual))
+        owned = apply_rows(diag_inv_local, current, gather_rows(residual))
         solved.append(owned)
-        pieces = ring_gather(owned)
+        pieces = gather_rows(owned)
         if current + 1 < supernodes:
             residual = rhs_group[current + 1] - apply_rows(sub_local, current, pieces)
             whole = assemble(pieces, order)

time: 182 us -> 183 us (level)
  waiting for transfers between devices: 84.6 us -> 75 us
  starting transfers between devices: 42.8 us -> 51.2 us
    ppermute x24 -> x0, waiting for transfers between devices: 68.2 us -> none  [ring_send(): return lax.ppermute(value, 'grp', pairs)]
    ppermute x9 -> x33, waiting for transfers between devices: 11.7 us -> 70.3 us  [send(): lax.ppermute(value, axis, [(i, (i + shift) % count) for i in range(count)])]
    ppermute x9 -> x33, starting transfers between devices: 10.4 us -> 47.7 us  [send(): lax.ppermute(value, axis, [(i, (i + shift) % count) for i in range(count)])]
    ppermute x24 -> x0, starting transfers between devices: 28.9 us -> none  [ring_send(): return lax.ppermute(value, 'grp', pairs)]
  transfers between devices with their start and end apart: 37 -> 37, of which waited for: 25 -> 23; matrix products, arithmetic and copies ran while one was open for 16% -> 15% of each run, Pallas kernels for 0% -> 0%
where the time goes in v4:
time: 183 us; the launch traced here: 182 us
  waiting for transfers between devices  75 us (41%)
  starting transfers between devices  51.2 us (28%)
  matrix products  31 us (17%)
  local copies, waits for them, and re-layouts  11.8 us (6%)
  other arithmetic  11 us (6%)
  between operations  1.94 us (1%)
    ppermute x33, waiting for transfers between devices, send(): lax.ppermute(value, axis, [(i, (i + shift) % count) for i in range(count)])  70.3 us
    ppermute x33, starting transfers between devices, send(): lax.ppermute(value, axis, [(i, (i + shift) % count) for i in range(count)])  47.7 us
    dot_general x28, matrix products, product(): jnp.dot(left, right, precision=high, preferred_element_type=jnp.float32)  17.4 us
    dot_general x9, matrix products, contract_last(): lax.dot_general(left, right, (((left.ndim - 1,), (right.ndim - 1,)), ((),...  7.11 us
  transfers between devices with their start and end apart: 37, of which 23 were waited for; matrix products, arithmetic and copies ran while one was open for 15% of the time, Pallas kernels for 0%

profile of v4, /device:TPU:0, one launch (start us, length us, event | category | flops | bytes accessed | tf_op | source)
XLA Modules:
  0.0 181.9 jit_solution(12016116556162543919)
XLA Ops:
  0.6 1.7 slice_bitcast_fusion
  2.4 4.0 %collective-permute-start.1 = (f32[256,128]{1,0:T(8,128)}, f32[256,128]{1,0:T(8,128)}, u32[]{:S(2)}, u32[]{:S(2)}) collective-permute-start(f32[256,128]{1,0:T(8,128)} %slice_bitcast_fusion), channel_id=1, source_target_pairs={{0,2},{1,3},{2,0},{3,1},{4,6},{5,7},{6,4},{7,5},{8,10},{9,11},{10,... | collective-permute-start | bytes 393224 | tf_op jit(solution)/shard_map/ppermute | solution.py:25
  6.4 1.6 collective-permute-start
  8.0 2.2 %collective-permute-start.2 = (f32[256,128]{1,0:T(8,128)}, f32[256,128]{1,0:T(8,128)S(1)}, u32[]{:S(2)}, u32[]{:S(2)}) collective-permute-start(f32[256,128]{1,0:T(8,128)} %slice_bitcast_fusion), channel_id=1, source_target_pairs={{0,3},{1,0},{2,1},{3,2},{4,7},{5,4},{6,5},{7,6},{8,11},{9,8},{10,9... | collective-permute-start | bytes 393224 | tf_op jit(solution)/shard_map/ppermute | solution.py:25
  12.1 1.3 fusion.90
  13.4 1.2 fusion.212
  15.3 1.4 convolution_add_fusion.15
  17.3 1.2 fusion.86
  18.6 1.3 constant_dynamic-update-slice_fusion.3
  19.9 2.1 %collective-permute-start.5 = (f32[256,128]{1,0:T(8,128)S(1)}, f32[256,128]{1,0:T(8,128)S(1)}, u32[]{:S(2)}, u32[]{:S(2)}) collective-permute-start(f32[256,128]{1,0:T(8,128)S(1)} %get-tuple-element.34), channel_id=1, source_target_pairs={{0,3},{1,0},{2,1},{3,2},{4,7},{5,4},{6,5},{7,6},{8,11},{9,8},{10,9... | collective-permute-start | bytes 393224 | tf_op jit(solution)/shard_map/ppermute | solution.py:25
  22.0 3.1 %collective-permute-start.4 = (f32[256,128]{1,0:T(8,128)S(1)}, f32[256,128]{1,0:T(8,128)S(1)}, u32[]{:S(2)}, u32[]{:S(2)}) collective-permute-start(f32[256,128]{1,0:T(8,128)S(1)} %get-tuple-element.34), channel_id=1, source_target_pairs={{0,2},{1,3},{2,0},{3,1},{4,6},{5,7},{6,4},{7,5},{8,10},{9,11},{10,... | collective-permute-start | bytes 393224 | tf_op jit(solution)/shard_map/ppermute | solution.py:25
  25.1 1.9 %collective-permute-start.3 = (f32[256,128]{1,0:T(8,128)S(1)}, f32[256,128]{1,0:T(8,128)S(1)}, u32[]{:S(2)}, u32[]{:S(2)}) collective-permute-start(f32[256,128]{1,0:T(8,128)S(1)} %get-tuple-element.34), channel_id=1, source_target_pairs={{0,1},{1,2},{2,3},{3,0},{4,5},{5,6},{6,7},{7,4},{8,9},{9,10},{10,1... | collective-permute-start | bytes 393224 | tf_op jit(solution)/shard_map/ppermute | solution.py:25
  27.3 8.3 %collective-permute-done.3 = f32[256,128]{1,0:T(8,128)S(1)} collective-permute-done((f32[256,128]{1,0:T(8,128)S(1)}, f32[256,128]{1,0:T(8,128)S(1)}, u32[]{:S(2)}, u32[]{:S(2)}) %collective-permute-start.3) | collective-permute-done | bytes 131104 | tf_op jit(solution)/shard_map/ppermute | solution.py:25
  37.1 1.2 fusion.15
  39.3 1.9 %collective-permute-start.6 = (f32[256,128]{1,0:T(8,128)S(1)}, f32[256,128]{1,0:T(8,128)S(1)}, u32[]{:S(2)}, u32[]{:S(2)}) collective-permute-start(f32[256,128]{1,0:T(8,128)S(1)} %fusion.15), channel_id=1, source_target_pairs={{0,1},{1,2},{2,3},{3,0},{4,5},{5,6},{6,7},{7,4},{8,9},{9,10},{10,1... | collective-permute-start | bytes 393224 | tf_op jit(solution)/shard_map/ppermute | solution.py:25
  41.3 8.5 %collective-permute-done.6 = f32[256,128]{1,0:T(8,128)S(1)} collective-permute-done((f32[256,128]{1,0:T(8,128)S(1)}, f32[256,128]{1,0:T(8,128)S(1)}, u32[]{:S(2)}, u32[]{:S(2)}) %collective-permute-start.6) | collective-permute-done | bytes 131104 | tf_op jit(solution)/shard_map/ppermute | solution.py:25
  51.7 2.5 %collective-permute-start.10 = (f32[256,128]{1,0:T(8,128)S(1)}, f32[256,128]{1,0:T(8,128)S(1)}, u32[]{:S(2)}, u32[]{:S(2)}) collective-permute-start(f32[256,128]{1,0:T(8,128)S(1)} %get-tuple-element.36), channel_id=1, source_target_pairs={{0,2},{1,3},{2,0},{3,1},{4,6},{5,7},{6,4},{7,5},{8,10},{9,11},{10,... | collective-permute-start | bytes 393224 | tf_op jit(solution)/shard_map/ppermute | solution.py:25
  54.2 1.9 %collective-permute-start.9 = (f32[256,128]{1,0:T(8,128)S(1)}, f32[256,128]{1,0:T(8,128)S(1)}, u32[]{:S(2)}, u32[]{:S(2)}) collective-permute-start(f32[256,128]{1,0:T(8,128)S(1)} %get-tuple-element.36), channel_id=1, source_target_pairs={{0,1},{1,2},{2,3},{3,0},{4,5},{5,6},{6,7},{7,4},{8,9},{9,10},{10,1... | collective-permute-start | bytes 393224 | tf_op jit(solution)/shard_map/ppermute | solution.py:25
  56.4 8.3 %collective-permute-done.9 = f32[256,128]{1,0:T(8,128)S(1)} collective-permute-done((f32[256,128]{1,0:T(8,128)S(1)}, f32[256,128]{1,0:T(8,128)S(1)}, u32[]{:S(2)}, u32[]{:S(2)}) %collective-permute-start.9) | collective-permute-done | bytes 131104 | tf_op jit(solution)/shard_map/ppermute | solution.py:25
  65.3 1.0 collective-permute-done.10
  67.7 1.9 %collective-permute-start.12 = (f32[256,128]{1,0:T(8,128)S(1)}, f32[256,128]{1,0:T(8,128)S(1)}, u32[]{:S(2)}, u32[]{:S(2)}) collective-permute-start(f32[256,128]{1,0:T(8,128)S(1)} %fusion.12), channel_id=1, source_target_pairs={{0,1},{1,2},{2,3},{3,0},{4,5},{5,6},{6,7},{7,4},{8,9},{9,10},{10,1... | collective-permute-start | bytes 393224 | tf_op jit(solution)/shard_map/ppermute | solution.py:25
  69.7 8.5 %collective-permute-done.12 = f32[256,128]{1,0:T(8,128)S(1)} collective-permute-done((f32[256,128]{1,0:T(8,128)S(1)}, f32[256,128]{1,0:T(8,128)S(1)}, u32[]{:S(2)}, u32[]{:S(2)}) %collective-permute-start.12) | collective-permute-done | bytes 131104 | tf_op jit(solution)/shard_map/ppermute | solution.py:25
  80.1 2.3 %collective-permute-start.16 = (f32[256,128]{1,0:T(8,128)S(1)}, f32[256,128]{1,0:T(8,128)S(1)}, u32[]{:S(2)}, u32[]{:S(2)}) collective-permute-start(f32[256,128]{1,0:T(8,128)S(1)} %get-tuple-element.38), channel_id=1, source_target_pairs={{0,2},{1,3},{2,0},{3,1},{4,6},{5,7},{6,4},{7,5},{8,10},{9,11},{10,... | collective-permute-start | bytes 393224 | tf_op jit(solution)/shard_map/ppermute | solution.py:25
  82.4 1.9 %collective-permute-start.15 = (f32[256,128]{1,0:T(8,128)S(1)}, f32[256,128]{1,0:T(8,128)S(1)}, u32[]{:S(2)}, u32[]{:S(2)}) collective-permute-start(f32[256,128]{1,0:T(8,128)S(1)} %get-tuple-element.38), channel_id=1, source_target_pairs={{0,1},{1,2},{2,3},{3,0},{4,5},{5,6},{6,7},{7,4},{8,9},{9,10},{10,1... | collective-permute-start | bytes 393224 | tf_op jit(solution)/shard_map/ppermute | solution.py:25
  84.7 8.3 %collective-permute-done.15 = f32[256,128]{1,0:T(8,128)S(1)} collective-permute-done((f32[256,128]{1,0:T(8,128)S(1)}, f32[256,128]{1,0:T(8,128)S(1)}, u32[]{:S(2)}, u32[]{:S(2)}) %collective-permute-start.15) | collective-permute-done | bytes 131104 | tf_op jit(solution)/shard_map/ppermute | solution.py:25
  96.1 2.0 %collective-permute-start.18 = (f32[256,128]{1,0:T(8,128)}, f32[256,128]{1,0:T(8,128)}, u32[]{:S(2)}, u32[]{:S(2)}) collective-permute-start(f32[256,128]{1,0:T(8,128)} %fusion.9), channel_id=1, source_target_pairs={{0,1},{1,2},{2,3},{3,0},{4,5},{5,6},{6,7},{7,4},{8,9},{9,10},{10,1... | collective-permute-start | bytes 393224 | tf_op jit(solution)/shard_map/ppermute | solution.py:25
  98.2 1.9 %fusion = f32[3,128,128]{1,2,0:T(8,128)} fusion(f32[1,1,3,128,1024]{4,3,2,1,0:T(8,128)S(1)} %copy-done.1, f32[1024,128]{1,0:T(8,128)S(1)} %constant_dynamic-update-slice_fusion, f32[1024,128]{1,0:T(8,128)S(1)} %constant_dynamic-update-slice_fusion.4, f32[1024,128]{1,0:T(8,128)S(1)} %constant_dynamic-update-slice_fusion.8, ...), kind=kOutput, calls=%fused_computation | convolution fusion | flops 303169536 | bytes 3342345 | tf_op jit(solution)/shard_map/mtk,mkr->rmt/dot_general | solution.py:153
  100.1 1.7 copy.26
  101.9 1.4 fusion.60
  103.3 3.7 %collective-permute-done.18 = f32[256,128]{1,0:T(8,128)} collective-permute-done((f32[256,128]{1,0:T(8,128)}, f32[256,128]{1,0:T(8,128)}, u32[]{:S(2)}, u32[]{:S(2)}) %collective-permute-start.18) | collective-permute-done | bytes 131104 | tf_op jit(solution)/shard_map/ppermute | solution.py:25
  107.0 1.3 convolution_add_fusion.3
  108.3 1.3 fusion.50
  109.6 1.3 fusion.7
  110.8 1.3 collective-permute-start.23
  112.1 2.0 %collective-permute-start.22 = (f32[256,128]{1,0:T(8,128)S(1)}, f32[256,128]{1,0:T(8,128)S(1)}, u32[]{:S(2)}, u32[]{:S(2)}) collective-permute-start(f32[256,128]{1,0:T(8,128)S(1)} %fusion.7), channel_id=1, source_target_pairs={{0,2},{1,3},{2,0},{3,1},{4,6},{5,7},{6,4},{7,5},{8,10},{9,11},{10,... | collective-permute-start | bytes 393224 | tf_op jit(solution)/shard_map/ppermute | solution.py:25
  114.2 1.9 %collective-permute-start.21 = (f32[256,128]{1,0:T(8,128)S(1)}, f32[256,128]{1,0:T(8,128)S(1)}, u32[]{:S(2)}, u32[]{:S(2)}) collective-permute-start(f32[256,128]{1,0:T(8,128)S(1)} %fusion.7), channel_id=1, source_target_pairs={{0,1},{1,2},{2,3},{3,0},{4,5},{5,6},{6,7},{7,4},{8,9},{9,10},{10,1... | collective-permute-start | bytes 393224 | tf_op jit(solution)/shard_map/ppermute | solution.py:25
  116.1 1.4 fusion.35
  117.5 7.1 %collective-permute-done.21 = f32[256,128]{1,0:T(8,128)S(1)} collective-permute-done((f32[256,128]{1,0:T(8,128)S(1)}, f32[256,128]{1,0:T(8,128)S(1)}, u32[]{:S(2)}, u32[]{:S(2)}) %collective-permute-start.21) | collective-permute-done | bytes 131104 | tf_op jit(solution)/shard_map/ppermute | solution.py:25
  127.4 1.7 collective-permute-done.24
  129.1 1.6 fusion.135
  130.6 1.5 collective-permute-start.25
  132.1 1.5 collective-permute-start.26
  134.8 1.4 bitcast_dynamic-update-slice_fusion
  136.7 2.4 %collective-permute-done.27 = f32[2,16,512]{2,1,0:T(8,128)} collective-permute-done((f32[2,16,512]{2,1,0:T(8,128)}, f32[2,16,512]{2,1,0:T(8,128)}, u32[]{:S(2)}, u32[]{:S(2)}) %collective-permute-start.27) | collective-permute-done | bytes 65568 | tf_op jit(solution)/shard_map/ppermute | solution.py:61
  141.6 1.7 reshape.281
  143.3 1.9 %convolution_bitcast_fusion = f32[16,16,128]{2,1,0:T(8,128)} fusion(f32[8,16,3,128]{3,2,1,0:T(4,128)} %reshape.281, f32[8,3]{0,1:T(4,128)S(1)} %bitcast.243), kind=kOutput, calls=%fused_computation.9 | convolution fusion | flops 4718976 | bytes 327776 | tf_op jit(solution)/shard_map/gmq,grmt->rqt/dot_general | solution.py:183
  145.3 1.6 reshape.282
  146.9 1.0 copy_subtract_fusion
  149.3 1.1 collective-permute-start.29
  150.4 2.9 %collective-permute-start.30 = (f32[16,1280]{1,0:T(8,128)}, f32[16,1280]{1,0:T(8,128)}, u32[]{:S(2)}, u32[]{:S(2)}) collective-permute-start(f32[16,1280]{1,0:T(8,128)} %get-tuple-element.28), channel_id=1, source_target_pairs={{0,3},{1,0},{2,1},{3,2},{4,7},{5,4},{6,5},{7,6},{8,11},{9,8},{10,9... | collective-permute-start | bytes 245768 | tf_op jit(solution)/shard_map/ppermute | solution.py:25
  153.3 2.7 %collective-permute-done.28 = f32[16,1280]{1,0:T(8,128)} collective-permute-done((f32[16,1280]{1,0:T(8,128)}, f32[16,1280]{1,0:T(8,128)}, u32[]{:S(2)}, u32[]{:S(2)}) %collective-permute-start.28) | collective-permute-done | bytes 81952 | tf_op jit(solution)/shard_map/ppermute | solution.py:25
  156.1 1.6 collective-permute-done.29
  157.7 1.0 fusion.131
  158.7 1.7 fusion.21
  160.4 2.7 %collective-permute-start.33 = (f32[16,256]{1,0:T(8,128)S(1)}, f32[16,256]{1,0:T(8,128)S(1)}, u32[]{:S(2)}, u32[]{:S(2)}) collective-permute-start(f32[16,256]{1,0:T(8,128)S(1)} %fusion.21), channel_id=1, source_target_pairs={{0,3},{1,0},{2,1},{3,2},{4,7},{5,4},{6,5},{7,6},{8,11},{9,8},{10,9... | collective-permute-start | bytes 49160 | tf_op jit(solution)/shard_map/ppermute | solution.py:25
  163.7 1.1 fusion.47
  164.9 4.0 %collective-permute-done.31 = f32[16,256]{1,0:T(8,128)S(1)} collective-permute-done((f32[16,256]{1,0:T(8,128)S(1)}, f32[16,256]{1,0:T(8,128)S(1)}, u32[]{:S(2)}, u32[]{:S(2)}) %collective-permute-start.31) | collective-permute-done | bytes 16416 | tf_op jit(solution)/shard_map/ppermute | solution.py:25
  168.9 1.1 convolution_add_fusion.18
  170.1 1.1 fusion.43
  171.3 1.1 slice_subtract_fusion
  172.9 1.7 maximum_bitcast_fusion
  175.2 2.0 %collective-permute-start.34 = (f32[16,256]{1,0:T(8,128)S(1)}, f32[16,256]{1,0:T(8,128)S(1)}, u32[]{:S(2)}, u32[]{:S(2)}) collective-permute-start(f32[16,256]{1,0:T(8,128)S(1)} %slice_subtract_fusion), channel_id=1, source_target_pairs={{0,1},{1,2},{2,3},{3,0},{4,5},{5,6},{6,7},{7,4},{8,9},{9,10},{10,1... | collective-permute-start | bytes 49160 | tf_op jit(solution)/shard_map/ppermute | solution.py:25
  177.4 1.9 %collective-permute-done.35 = f32[16,256]{1,0:T(8,128)S(1)} collective-permute-done((f32[16,256]{1,0:T(8,128)S(1)}, f32[16,256]{1,0:T(8,128)S(1)}, u32[]{:S(2)}, u32[]{:S(2)}) %collective-permute-start.35) | collective-permute-done | bytes 16416 | tf_op jit(solution)/shard_map/ppermute | solution.py:25
  179.4 1.3 collective-permute-done.34
  (109 shorter events, 26.3 us)
Async XLA Ops:
  0.6 26.4 %copy-start = (f32[1,3,256,1024]{3,2,1,0:T(8,128)S(1)}, f32[1,3,256,1024]{3,2,1,0:T(8,128)}, u32[]{:S(2)}) copy-start(f32[1,3,256,1024]{3,2,1,0:T(8,128)} %param.14) | copy-start | bytes 9437188
  2.4 16.2 %collective-permute-start.1 = (f32[256,128]{1,0:T(8,128)}, f32[256,128]{1,0:T(8,128)}, u32[]{:S(2)}, u32[]{:S(2)}) collective-permute-start(f32[256,128]{1,0:T(8,128)} %slice_bitcast_fusion), channel_id=1, source_target_pairs={{0,2},{1,3},{2,0},{3,1},{4,6},{5,7},{6,4},{7,5},{8,10},{9,11},{10,... | collective-permute-start | bytes 393224 | tf_op jit(solution)/shard_map/ppermute | solution.py:25
  6.4 8.9 %collective-permute-start = (f32[256,128]{1,0:T(8,128)}, f32[256,128]{1,0:T(8,128)S(1)}, u32[]{:S(2)}, u32[]{:S(2)}) collective-permute-start(f32[256,128]{1,0:T(8,128)} %slice_bitcast_fusion), channel_id=1, source_target_pairs={{0,1},{1,2},{2,3},{3,0},{4,5},{5,6},{6,7},{7,4},{8,9},{9,10},{10,1... | collective-permute-start | bytes 393224 | tf_op jit(solution)/shard_map/ppermute | solution.py:25
  8.0 9.3 %collective-permute-start.2 = (f32[256,128]{1,0:T(8,128)}, f32[256,128]{1,0:T(8,128)S(1)}, u32[]{:S(2)}, u32[]{:S(2)}) collective-permute-start(f32[256,128]{1,0:T(8,128)} %slice_bitcast_fusion), channel_id=1, source_target_pairs={{0,3},{1,0},{2,1},{3,2},{4,7},{5,4},{6,5},{7,6},{8,11},{9,8},{10,9... | collective-permute-start | bytes 393224 | tf_op jit(solution)/shard_map/ppermute | solution.py:25
  14.6 23.8 %copy-start.3 = (f32[1,4,256,1024]{3,2,1,0:T(8,128)S(1)}, f32[1,4,256,1024]{3,2,1,0:T(8,128)}, u32[]{:S(2)}) copy-start(f32[1,4,256,1024]{3,2,1,0:T(8,128)} %param.13) | copy-start | bytes 12582916
  19.9 16.0 %collective-permute-start.5 = (f32[256,128]{1,0:T(8,128)S(1)}, f32[256,128]{1,0:T(8,128)S(1)}, u32[]{:S(2)}, u32[]{:S(2)}) collective-permute-start(f32[256,128]{1,0:T(8,128)S(1)} %get-tuple-element.34), channel_id=1, source_target_pairs={{0,3},{1,0},{2,1},{3,2},{4,7},{5,4},{6,5},{7,6},{8,11},{9,8},{10,9... | collective-permute-start | bytes 393224 | tf_op jit(solution)/shard_map/ppermute | solution.py:25
  22.0 15.1 %collective-permute-start.4 = (f32[256,128]{1,0:T(8,128)S(1)}, f32[256,128]{1,0:T(8,128)S(1)}, u32[]{:S(2)}, u32[]{:S(2)}) collective-permute-start(f32[256,128]{1,0:T(8,128)S(1)} %get-tuple-element.34), channel_id=1, source_target_pairs={{0,2},{1,3},{2,0},{3,1},{4,6},{5,7},{6,4},{7,5},{8,10},{9,11},{10,... | collective-permute-start | bytes 393224 | tf_op jit(solution)/shard_map/ppermute | solution.py:25
  25.1 10.5 %collective-permute-start.3 = (f32[256,128]{1,0:T(8,128)S(1)}, f32[256,128]{1,0:T(8,128)S(1)}, u32[]{:S(2)}, u32[]{:S(2)}) collective-permute-start(f32[256,128]{1,0:T(8,128)S(1)} %get-tuple-element.34), channel_id=1, source_target_pairs={{0,1},{1,2},{2,3},{3,0},{4,5},{5,6},{6,7},{7,4},{8,9},{9,10},{10,1... | collective-permute-start | bytes 393224 | tf_op jit(solution)/shard_map/ppermute | solution.py:25
  36.2 30.1 %copy-start.6 = (f32[1,4,256,128]{3,2,1,0:T(8,128)S(1)}, f32[1,4,256,128]{3,2,1,0:T(8,128)}, u32[]{:S(2)}) copy-start(f32[1,4,256,128]{3,2,1,0:T(8,128)} %param.12) | copy-start | bytes 1572868
  38.6 11.5 %collective-permute-start.8 = (f32[256,128]{1,0:T(8,128)S(1)}, f32[256,128]{1,0:T(8,128)S(1)}, u32[]{:S(2)}, u32[]{:S(2)}) collective-permute-start(f32[256,128]{1,0:T(8,128)S(1)} %fusion.15), channel_id=1, source_target_pairs={{0,3},{1,0},{2,1},{3,2},{4,7},{5,4},{6,5},{7,6},{8,11},{9,8},{10,9... | collective-permute-start | bytes 393224 | tf_op jit(solution)/shard_map/ppermute | solution.py:25
  38.7 12.7 %collective-permute-start.7 = (f32[256,128]{1,0:T(8,128)S(1)}, f32[256,128]{1,0:T(8,128)S(1)}, u32[]{:S(2)}, u32[]{:S(2)}) collective-permute-start(f32[256,128]{1,0:T(8,128)S(1)} %fusion.15), channel_id=1, source_target_pairs={{0,2},{1,3},{2,0},{3,1},{4,6},{5,7},{6,4},{7,5},{8,10},{9,11},{10,... | collective-permute-start | bytes 393224 | tf_op jit(solution)/shard_map/ppermute | solution.py:25
  39.3 10.5 %collective-permute-start.6 = (f32[256,128]{1,0:T(8,128)S(1)}, f32[256,128]{1,0:T(8,128)S(1)}, u32[]{:S(2)}, u32[]{:S(2)}) collective-permute-start(f32[256,128]{1,0:T(8,128)S(1)} %fusion.15), channel_id=1, source_target_pairs={{0,1},{1,2},{2,3},{3,0},{4,5},{5,6},{6,7},{7,4},{8,9},{9,10},{10,1... | collective-permute-start | bytes 393224 | tf_op jit(solution)/shard_map/ppermute | solution.py:25
  51.7 13.3 %collective-permute-start.11 = (f32[256,128]{1,0:T(8,128)S(1)}, f32[256,128]{1,0:T(8,128)S(1)}, u32[]{:S(2)}, u32[]{:S(2)}) collective-permute-start(f32[256,128]{1,0:T(8,128)S(1)} %get-tuple-element.36), channel_id=1, source_target_pairs={{0,3},{1,0},{2,1},{3,2},{4,7},{5,4},{6,5},{7,6},{8,11},{9,8},{10,9... | collective-permute-start | bytes 393224 | tf_op jit(solution)/shard_map/ppermute | solution.py:25
  51.7 14.5 %collective-permute-start.10 = (f32[256,128]{1,0:T(8,128)S(1)}, f32[256,128]{1,0:T(8,128)S(1)}, u32[]{:S(2)}, u32[]{:S(2)}) collective-permute-start(f32[256,128]{1,0:T(8,128)S(1)} %get-tuple-element.36), channel_id=1, source_target_pairs={{0,2},{1,3},{2,0},{3,1},{4,6},{5,7},{6,4},{7,5},{8,10},{9,11},{10,... | collective-permute-start | bytes 393224 | tf_op jit(solution)/shard_map/ppermute | solution.py:25
  54.2 10.5 %collective-permute-start.9 = (f32[256,128]{1,0:T(8,128)S(1)}, f32[256,128]{1,0:T(8,128)S(1)}, u32[]{:S(2)}, u32[]{:S(2)}) collective-permute-start(f32[256,128]{1,0:T(8,128)S(1)} %get-tuple-element.36), channel_id=1, source_target_pairs={{0,1},{1,2},{2,3},{3,0},{4,5},{5,6},{6,7},{7,4},{8,9},{9,10},{10,1... | collective-permute-start | bytes 393224 | tf_op jit(solution)/shard_map/ppermute | solution.py:25
  66.8 11.6 %collective-permute-start.14 = (f32[256,128]{1,0:T(8,128)S(1)}, f32[256,128]{1,0:T(8,128)S(1)}, u32[]{:S(2)}, u32[]{:S(2)}) collective-permute-start(f32[256,128]{1,0:T(8,128)S(1)} %fusion.12), channel_id=1, source_target_pairs={{0,3},{1,0},{2,1},{3,2},{4,7},{5,4},{6,5},{7,6},{8,11},{9,8},{10,9... | collective-permute-start | bytes 393224 | tf_op jit(solution)/shard_map/ppermute | solution.py:25
  66.9 12.8 %collective-permute-start.13 = (f32[256,128]{1,0:T(8,128)S(1)}, f32[256,128]{1,0:T(8,128)S(1)}, u32[]{:S(2)}, u32[]{:S(2)}) collective-permute-start(f32[256,128]{1,0:T(8,128)S(1)} %fusion.12), channel_id=1, source_target_pairs={{0,2},{1,3},{2,0},{3,1},{4,6},{5,7},{6,4},{7,5},{8,10},{9,11},{10,... | collective-permute-start | bytes 393224 | tf_op jit(solution)/shard_map/ppermute | solution.py:25
  67.7 10.5 %collective-permute-start.12 = (f32[256,128]{1,0:T(8,128)S(1)}, f32[256,128]{1,0:T(8,128)S(1)}, u32[]{:S(2)}, u32[]{:S(2)}) collective-permute-start(f32[256,128]{1,0:T(8,128)S(1)} %fusion.12), channel_id=1, source_target_pairs={{0,1},{1,2},{2,3},{3,0},{4,5},{5,6},{6,7},{7,4},{8,9},{9,10},{10,1... | collective-permute-start | bytes 393224 | tf_op jit(solution)/shard_map/ppermute | solution.py:25
  69.7 28.5 %copy-start.1 = (f32[1,1,3,128,1024]{4,3,2,1,0:T(8,128)S(1)}, f32[1,1,3,128,1024]{4,3,2,1,0:T(8,128)}, u32[]{:S(2)}) copy-start(f32[1,1,3,128,1024]{4,3,2,1,0:T(8,128)} %param.15) | copy-start | bytes 4718596
  80.0 13.2 %collective-permute-start.17 = (f32[256,128]{1,0:T(8,128)S(1)}, f32[256,128]{1,0:T(8,128)S(1)}, u32[]{:S(2)}, u32[]{:S(2)}) collective-permute-start(f32[256,128]{1,0:T(8,128)S(1)} %get-tuple-element.38), channel_id=1, source_target_pairs={{0,3},{1,0},{2,1},{3,2},{4,7},{5,4},{6,5},{7,6},{8,11},{9,8},{10,9... | collective-permute-start | bytes 393224 | tf_op jit(solution)/shard_map/ppermute | solution.py:25
  80.1 14.4 %collective-permute-start.16 = (f32[256,128]{1,0:T(8,128)S(1)}, f32[256,128]{1,0:T(8,128)S(1)}, u32[]{:S(2)}, u32[]{:S(2)}) collective-permute-start(f32[256,128]{1,0:T(8,128)S(1)} %get-tuple-element.38), channel_id=1, source_target_pairs={{0,2},{1,3},{2,0},{3,1},{4,6},{5,7},{6,4},{7,5},{8,10},{9,11},{10,... | collective-permute-start | bytes 393224 | tf_op jit(solution)/shard_map/ppermute | solution.py:25
  82.4 10.5 %collective-permute-start.15 = (f32[256,128]{1,0:T(8,128)S(1)}, f32[256,128]{1,0:T(8,128)S(1)}, u32[]{:S(2)}, u32[]{:S(2)}) collective-permute-start(f32[256,128]{1,0:T(8,128)S(1)} %get-tuple-element.38), channel_id=1, source_target_pairs={{0,1},{1,2},{2,3},{3,0},{4,5},{5,6},{6,7},{7,4},{8,9},{9,10},{10,1... | collective-permute-start | bytes 393224 | tf_op jit(solution)/shard_map/ppermute | solution.py:25
  95.4 12.9 %collective-permute-start.20 = (f32[256,128]{1,0:T(8,128)}, f32[256,128]{1,0:T(8,128)}, u32[]{:S(2)}, u32[]{:S(2)}) collective-permute-start(f32[256,128]{1,0:T(8,128)} %fusion.9), channel_id=1, source_target_pairs={{0,3},{1,0},{2,1},{3,2},{4,7},{5,4},{6,5},{7,6},{8,11},{9,8},{10,9... | collective-permute-start | bytes 393224 | tf_op jit(solution)/shard_map/ppermute | solution.py:25
  95.4 14.2 %collective-permute-start.19 = (f32[256,128]{1,0:T(8,128)}, f32[256,128]{1,0:T(8,128)}, u32[]{:S(2)}, u32[]{:S(2)}) collective-permute-start(f32[256,128]{1,0:T(8,128)} %fusion.9), channel_id=1, source_target_pairs={{0,2},{1,3},{2,0},{3,1},{4,6},{5,7},{6,4},{7,5},{8,10},{9,11},{10,... | collective-permute-start | bytes 393224 | tf_op jit(solution)/shard_map/ppermute | solution.py:25
  96.1 10.9 %collective-permute-start.18 = (f32[256,128]{1,0:T(8,128)}, f32[256,128]{1,0:T(8,128)}, u32[]{:S(2)}, u32[]{:S(2)}) collective-permute-start(f32[256,128]{1,0:T(8,128)} %fusion.9), channel_id=1, source_target_pairs={{0,1},{1,2},{2,3},{3,0},{4,5},{5,6},{6,7},{7,4},{8,9},{9,10},{10,1... | collective-permute-start | bytes 393224 | tf_op jit(solution)/shard_map/ppermute | solution.py:25
  100.1 26.1 %copy-start.9 = (pred[384]{0:T(512)(128)(4,1)S(1)}, pred[384]{0:T(512)(128)(4,1)}, u32[]{:S(2)}) copy-start(pred[384]{0:T(512)(128)(4,1)} %broadcast_bitcast_fusion) | copy-start | bytes 1156
  101.9 22.8 %copy-start.2 = (f32[1,1,3,128,1024]{4,3,2,1,0:T(8,128)S(1)}, f32[1,1,3,128,1024]{4,3,2,1,0:T(8,128)}, u32[]{:S(2)}) copy-start(f32[1,1,3,128,1024]{4,3,2,1,0:T(8,128)} %param.15) | copy-start | bytes 4718596
  101.9 24.3 %copy-start.7 = (f32[128,384]{1,0:T(8,128)S(1)}, f32[128,384]{1,0:T(8,128)}, u32[]{:S(2)}) copy-start(f32[128,384]{1,0:T(8,128)} %copy.26) | copy-start | bytes 589828
  110.8 5.3 %copy-start.5 = (f32[256,128]{1,0:T(8,128)}, f32[256,128]{1,0:T(8,128)S(1)}, u32[]{:S(2)}) copy-start(f32[256,128]{1,0:T(8,128)S(1)} %fusion.7) | copy-start | bytes 393220
  110.8 14.3 %collective-permute-start.23 = (f32[256,128]{1,0:T(8,128)S(1)}, f32[256,128]{1,0:T(8,128)S(1)}, u32[]{:S(2)}, u32[]{:S(2)}) collective-permute-start(f32[256,128]{1,0:T(8,128)S(1)} %fusion.7), channel_id=1, source_target_pairs={{0,3},{1,0},{2,1},{3,2},{4,7},{5,4},{6,5},{7,6},{8,11},{9,8},{10,9... | collective-permute-start | bytes 393224 | tf_op jit(solution)/shard_map/ppermute | solution.py:25
  112.1 14.1 %collective-permute-start.22 = (f32[256,128]{1,0:T(8,128)S(1)}, f32[256,128]{1,0:T(8,128)S(1)}, u32[]{:S(2)}, u32[]{:S(2)}) collective-permute-start(f32[256,128]{1,0:T(8,128)S(1)} %fusion.7), channel_id=1, source_target_pairs={{0,2},{1,3},{2,0},{3,1},{4,6},{5,7},{6,4},{7,5},{8,10},{9,11},{10,... | collective-permute-start | bytes 393224 | tf_op jit(solution)/shard_map/ppermute | solution.py:25
  114.2 10.5 %collective-permute-start.21 = (f32[256,128]{1,0:T(8,128)S(1)}, f32[256,128]{1,0:T(8,128)S(1)}, u32[]{:S(2)}, u32[]{:S(2)}) collective-permute-start(f32[256,128]{1,0:T(8,128)S(1)} %fusion.7), channel_id=1, source_target_pairs={{0,1},{1,2},{2,3},{3,0},{4,5},{5,6},{6,7},{7,4},{8,9},{9,10},{10,1... | collective-permute-start | bytes 393224 | tf_op jit(solution)/shard_map/ppermute | solution.py:25
  127.4 1.7 collective-permute-start.24
  130.6 5.5 %collective-permute-start.25 = (f32[2,16,512]{2,1,0:T(8,128)}, f32[2,16,512]{2,1,0:T(8,128)}, u32[]{:S(2)}, u32[]{:S(2)}) collective-permute-start(f32[2,16,512]{2,1,0:T(8,128)} %get-tuple-element.15), channel_id=1, source_target_pairs={{0,8},{4,12},{8,0},{12,4},{16,24},{20,28},{24,16},{28,20},{1,9},{5... | collective-permute-start | bytes 196616 | tf_op jit(solution)/shard_map/ppermute | solution.py:61
  132.1 4.6 %collective-permute-start.26 = (f32[2,16,512]{2,1,0:T(8,128)}, f32[2,16,512]{2,1,0:T(8,128)}, u32[]{:S(2)}, u32[]{:S(2)}) collective-permute-start(f32[2,16,512]{2,1,0:T(8,128)} %get-tuple-element.16), channel_id=1, source_target_pairs={{0,16},{4,20},{8,24},{12,28},{16,0},{20,4},{24,8},{28,12},{1,17},{... | collective-permute-start | bytes 196616 | tf_op jit(solution)/shard_map/ppermute | solution.py:61
  133.7 5.5 %collective-permute-start.27 = (f32[2,16,512]{2,1,0:T(8,128)}, f32[2,16,512]{2,1,0:T(8,128)}, u32[]{:S(2)}, u32[]{:S(2)}) collective-permute-start(f32[2,16,512]{2,1,0:T(8,128)} %get-tuple-element.17), channel_id=1, source_target_pairs={{0,24},{4,28},{8,16},{12,20},{16,8},{20,12},{24,0},{28,4},{1,25},{... | collective-permute-start | bytes 196616 | tf_op jit(solution)/shard_map/ppermute | solution.py:61
  147.9 0.6 copy-start.8
  149.3 6.8 %collective-permute-start.28 = (f32[16,1280]{1,0:T(8,128)}, f32[16,1280]{1,0:T(8,128)}, u32[]{:S(2)}, u32[]{:S(2)}) collective-permute-start(f32[16,1280]{1,0:T(8,128)} %get-tuple-element.26), channel_id=1, source_target_pairs={{0,1},{1,2},{2,3},{3,0},{4,5},{5,6},{6,7},{7,4},{8,9},{9,10},{10,1... | collective-permute-start | bytes 245768 | tf_op jit(solution)/shard_map/ppermute | solution.py:25
  149.3 8.4 %collective-permute-start.29 = (f32[16,1280]{1,0:T(8,128)}, f32[16,1280]{1,0:T(8,128)}, u32[]{:S(2)}, u32[]{:S(2)}) collective-permute-start(f32[16,1280]{1,0:T(8,128)} %get-tuple-element.27), channel_id=1, source_target_pairs={{0,2},{1,3},{2,0},{3,1},{4,6},{5,7},{6,4},{7,5},{8,10},{9,11},{10,... | collective-permute-start | bytes 245768 | tf_op jit(solution)/shard_map/ppermute | solution.py:25
  150.4 7.3 %collective-permute-start.30 = (f32[16,1280]{1,0:T(8,128)}, f32[16,1280]{1,0:T(8,128)}, u32[]{:S(2)}, u32[]{:S(2)}) collective-permute-start(f32[16,1280]{1,0:T(8,128)} %get-tuple-element.28), channel_id=1, source_target_pairs={{0,3},{1,0},{2,1},{3,2},{4,7},{5,4},{6,5},{7,6},{8,11},{9,8},{10,9... | collective-permute-start | bytes 245768 | tf_op jit(solution)/shard_map/ppermute | solution.py:25
  153.3 23.9 %copy-start.4 = (f32[2,256,1024]{2,1,0:T(8,128)S(1)}, f32[2,256,1024]{2,1,0:T(8,128)}, u32[]{:S(2)}) copy-start(f32[2,256,1024]{2,1,0:T(8,128)} %param.20) | copy-start | bytes 6291460
  160.4 9.7 %collective-permute-start.33 = (f32[16,256]{1,0:T(8,128)S(1)}, f32[16,256]{1,0:T(8,128)S(1)}, u32[]{:S(2)}, u32[]{:S(2)}) collective-permute-start(f32[16,256]{1,0:T(8,128)S(1)} %fusion.21), channel_id=1, source_target_pairs={{0,3},{1,0},{2,1},{3,2},{4,7},{5,4},{6,5},{7,6},{8,11},{9,8},{10,9... | collective-permute-start | bytes 49160 | tf_op jit(solution)/shard_map/ppermute | solution.py:25
  163.1 8.2 %collective-permute-start.32 = (f32[16,256]{1,0:T(8,128)S(1)}, f32[16,256]{1,0:T(8,128)S(1)}, u32[]{:S(2)}, u32[]{:S(2)}) collective-permute-start(f32[16,256]{1,0:T(8,128)S(1)} %fusion.21), channel_id=1, source_target_pairs={{0,2},{1,3},{2,0},{3,1},{4,6},{5,7},{6,4},{7,5},{8,10},{9,11},{10,... | collective-permute-start | bytes 49160 | tf_op jit(solution)/shard_map/ppermute | solution.py:25
  163.4 5.5 %collective-permute-start.31 = (f32[16,256]{1,0:T(8,128)S(1)}, f32[16,256]{1,0:T(8,128)S(1)}, u32[]{:S(2)}, u32[]{:S(2)}) collective-permute-start(f32[16,256]{1,0:T(8,128)S(1)} %fusion.21), channel_id=1, source_target_pairs={{0,1},{1,2},{2,3},{3,0},{4,5},{5,6},{6,7},{7,4},{8,9},{9,10},{10,1... | collective-permute-start | bytes 49160 | tf_op jit(solution)/shard_map/ppermute | solution.py:25
  172.5 4.7 %collective-permute-start.36 = (f32[16,256]{1,0:T(8,128)S(1)}, f32[16,256]{1,0:T(8,128)S(1)}, u32[]{:S(2)}, u32[]{:S(2)}) collective-permute-start(f32[16,256]{1,0:T(8,128)S(1)} %slice_subtract_fusion), channel_id=1, source_target_pairs={{0,3},{1,0},{2,1},{3,2},{4,7},{5,4},{6,5},{7,6},{8,11},{9,8},{10,9... | collective-permute-start | bytes 49160 | tf_op jit(solution)/shard_map/ppermute | solution.py:25
  174.6 4.6 %collective-permute-start.35 = (f32[16,256]{1,0:T(8,128)S(1)}, f32[16,256]{1,0:T(8,128)S(1)}, u32[]{:S(2)}, u32[]{:S(2)}) collective-permute-start(f32[16,256]{1,0:T(8,128)S(1)} %slice_subtract_fusion), channel_id=1, source_target_pairs={{0,2},{1,3},{2,0},{3,1},{4,6},{5,7},{6,4},{7,5},{8,10},{9,11},{10,... | collective-permute-start | bytes 49160 | tf_op jit(solution)/shard_map/ppermute | solution.py:25
  175.2 5.5 %collective-permute-start.34 = (f32[16,256]{1,0:T(8,128)S(1)}, f32[16,256]{1,0:T(8,128)S(1)}, u32[]{:S(2)}, u32[]{:S(2)}) collective-permute-start(f32[16,256]{1,0:T(8,128)S(1)} %slice_subtract_fusion), channel_id=1, source_target_pairs={{0,1},{1,2},{2,3},{3,0},{4,5},{5,6},{6,7},{7,4},{8,9},{9,10},{10,1... | collective-permute-start | bytes 49160 | tf_op jit(solution)/shard_map/ppermute | solution.py:25

commit v5 on v4

--- a/solution.py
+++ b/solution.py
@@ -4,10 +4,6 @@
 from jax.sharding import PartitionSpec as P
 
 high = lax.Precision.HIGH
-
-
-def product(left, right):
-    return jnp.dot(left, right, precision=high, preferred_element_type=jnp.float32)
 
 
 def contract_last(left, right):
@@ -28,7 +24,7 @@
 def gather_rows(value):
     members = lax.axis_size("grp")
     me = lax.axis_index("grp")
-    rows = value.shape[0]
+    rows = value.shape[1]
     pieces = [(me * rows, value)]
     for shift in range(1, members):
         owner = lax.rem(me - shift + members, members)
@@ -46,9 +42,16 @@
 def apply_rows(factor, index, pieces):
     total = None
     for offset, piece in pieces:
-        term = product(columns_of(factor, index, offset, piece.shape[0]), piece)
+        term = contract_last(piece, columns_of(factor, index, offset, piece.shape[1]))
         total = term if total is None else total + term
     return total
+
+
+def assemble(pieces, order):
+    whole = jnp.zeros((pieces[0][1].shape[0], order), jnp.float32)
+    for offset, piece in pieces:
+        whole = lax.dynamic_update_slice_in_dim(whole, piece, offset, 1)
+    return whole
 
 
 def swap(value, axis, distance, block):
@@ -88,26 +91,6 @@
     return jnp.concatenate(parts, axis=0)
 
 
-def apply_wide(factor, index, portion):
-    members = lax.axis_size("grp")
-    me = lax.axis_index("grp")
-    rows = portion.shape[-1]
-    total = None
-    for shift in range(members):
-        piece = portion if shift == 0 else send(portion, "grp", shift)
-        owner = lax.rem(me - shift + members, members)
-        term = contract_last(piece, columns_of(factor, index, owner * rows, rows))
-        total = term if total is None else total + term
-    return total
-
-
-def assemble(pieces, order):
-    whole = jnp.zeros((order, pieces[0][1].shape[1]), jnp.float32)
-    for offset, piece in pieces:
-        whole = lax.dynamic_update_slice_in_dim(whole, piece, offset, 0)
-    return whole
-
-
 def on_device(
     rhs_local,
     diag_inv_local,
@@ -138,33 +121,39 @@
     ).astype(jnp.float32)
     sources = tile_source[0, 0]
 
+    streams = 2 if rhs_count % 16 == 0 else 1
+    depth = rhs_count // streams
+    rhs_wide = jnp.swapaxes(rhs_group, 1, 2)
+    split = [rhs_wide[:, i * depth : (i + 1) * depth] for i in range(streams)]
     solved = []
-    residual = rhs_group[0]
-    chosen = jnp.zeros((slots, order, rhs_count), jnp.float32)
+    residuals = [portion[0] for portion in split]
+    chosen = [jnp.zeros((slots, depth, order), jnp.float32) for _ in range(streams)]
     for current in range(supernodes):
-        owned = apply_rows(diag_inv_local, current, gather_rows(residual))
-        solved.append(owned)
-        pieces = gather_rows(owned)
+        owned = [apply_rows(diag_inv_local, current, gather_rows(r)) for r in residuals]
+        solved.append(jnp.transpose(jnp.concatenate(owned, axis=0)))
+        held = [gather_rows(value) for value in owned]
         if current + 1 < supernodes:
-            residual = rhs_group[current + 1] - apply_rows(sub_local, current, pieces)
-            whole = assemble(pieces, order)
-            chosen = jnp.where((sources == current)[:, None, None], whole[None], chosen)
-
-    early = jnp.einsum(
-        "mtk,mkr->rmt", tiles_mine, chosen, precision=high, preferred_element_type=jnp.float32
-    ).reshape(rhs_count, slots * tile_rows)
+            residuals = [
+                portion[current + 1] - apply_rows(sub_local, current, pieces)
+                for portion, pieces in zip(split, held)
+            ]
+            chosen = [
+                jnp.where((sources == current)[:, None, None], assemble(pieces, order)[None], old)
+                for pieces, old in zip(held, chosen)
+            ]
+
     flat_tiles = tiles_mine.reshape(slots * tile_rows, order)
-    late = None
-    for offset, piece in pieces:
-        columns = lax.dynamic_slice_in_dim(flat_tiles, offset, piece.shape[0], 1)
-        term = lax.dot_general(
-            piece,
-            columns,
-            (((0,), (1,)), ((), ())),
-            precision=high,
-            preferred_element_type=jnp.float32,
+    early = []
+    late = []
+    for pieces, picked in zip(held, chosen):
+        early.append(
+            jnp.concatenate(
+                [contract_last(picked[m], tiles_mine[m]) for m in range(slots)], axis=1
+            )
         )
-        late = term if late is None else late + term
+        late.append(apply_rows(flat_tiles[None], 0, pieces))
+    early = jnp.concatenate(early, axis=0)
+    late = jnp.concatenate(late, axis=0)
     is_late = jnp.repeat(sources == supernodes - 1, tile_rows)
     terms = jnp.where(is_late[None, :], late, early)
     tag = jnp.zeros((tile_rows,), jnp.float32).at[:slots].set(blocks)
@@ -205,8 +194,10 @@
     solutions = [contract_last(total[:, :order], diag_inv_anc[0])]
     for ancestor in range(1, ancestors):
         begin = order + (ancestor - 1) * rows
-        residual = total[:, begin : begin + rows] - apply_wide(sub_anc, ancestor - 1, solutions[-1])
-        solutions.append(apply_wide(diag_inv_anc, ancestor, residual))
+        residual = total[:, begin : begin + rows] - apply_rows(
+            sub_anc, ancestor - 1, gather_rows(solutions[-1])
+        )
+        solutions.append(apply_rows(diag_inv_anc, ancestor, gather_rows(residual)))
     solutions = jnp.stack([jnp.transpose(s) for s in solutions])
     return (jnp.stack(solved)[None], solutions)
 

time: 183 us -> 169 us (0.923)
  waiting for transfers between devices: 75 us -> 23.6 us
  starting transfers between devices: 51.2 us -> 86.2 us
  matrix products: 31 us -> 36.6 us
  other arithmetic: 11 us -> 7.1 us
    ppermute x33 -> x57, waiting for transfers between devices: 70.3 us -> 20.6 us  [send(): lax.ppermute(value, axis, [(i, (i + shift) % count) for i in range(count)])]
    ppermute x33 -> x57, starting transfers between devices: 47.7 us -> 82.6 us  [send(): lax.ppermute(value, axis, [(i, (i + shift) % count) for i in range(count)])]
    dot_general x9 -> x79, matrix products: 7.11 us -> 35.6 us  [contract_last(): lax.dot_general(left, right, (((left.ndim - 1,), (right.ndim - 1,)), ((),...]
    dot_general x33 -> x0, matrix products: 21.9 us -> none  [the longest x28 17.4 us: product(): jnp.dot(left, right, precision=high, preferred_element_type=jnp.float32)]
    unnamed x20 -> x28, local copies, waits for them, and re-layouts: 0.64 us -> 4.85 us
    another operation x0 -> x4, other arithmetic: none -> 1.98 us  [on_device(): return (jnp.stack(solved)[None], solutions)]
  transfers between devices with their start and end apart: 37 -> 61, of which waited for: 23 -> 17; matrix products, arithmetic and copies ran while one was open for 15% -> 24% of each run, Pallas kernels for 0% -> 0%
where the time goes in v5:
time: 169 us; the launch traced here: 168 us
  starting transfers between devices  86.2 us (51%)
  matrix products  36.6 us (22%)
  waiting for transfers between devices  23.6 us (14%)
  local copies, waits for them, and re-layouts  12.1 us (7%)
  other arithmetic  7.1 us (4%)
  between operations  2.66 us (2%)
    ppermute x57, starting transfers between devices, send(): lax.ppermute(value, axis, [(i, (i + shift) % count) for i in range(count)])  82.6 us
    dot_general x79, matrix products, contract_last(): lax.dot_general(left, right, (((left.ndim - 1,), (right.ndim - 1,)), ((),...  35.6 us
    ppermute x57, waiting for transfers between devices, send(): lax.ppermute(value, axis, [(i, (i + shift) % count) for i in range(count)])  20.6 us
    unnamed x28, local copies, waits for them, and re-layouts  4.85 us
    ppermute x3, starting transfers between devices, swap(): return lax.ppermute(value, axis, pairs)  3.55 us
  transfers between devices with their start and end apart: 61, of which 17 were waited for; matrix products, arithmetic and copies ran while one was open for 24% of the time, Pallas kernels for 0%

profile of v5, /device:TPU:0, one launch (start us, length us, event | category | flops | bytes accessed | tf_op | source)
XLA Modules:
  0.0 168.3 jit_solution(7032657943740265370)
XLA Ops:
  0.6 2.2 %copy.28 = f32[1,4,256,128]{2,3,1,0:T(8,128)} copy(f32[1,4,256,128]{3,2,1,0:T(8,128)} %param.12) | data formatting | bytes 1048576 | tf_op args[0]
  2.8 1.5 slice_bitcast_fusion.20
  4.3 5.0 %collective-permute-start.5 = (f32[64,256]{1,0:T(8,128)}, f32[64,256]{1,0:T(8,128)}, u32[]{:S(2)}, u32[]{:S(2)}) collective-permute-start(f32[64,256]{1,0:T(8,128)} %get-tuple-element.21), channel_id=1, source_target_pairs={{0,3},{1,0},{2,1},{3,2},{4,7},{5,4},{6,5},{7,6},{8,11},{9,8},{10,9... | collective-permute-start | bytes 196616 | tf_op jit(solution)/shard_map/ppermute | solution.py:21
  9.4 1.0 collective-permute-start.4
  10.4 2.8 %collective-permute-start.2 = (f32[64,256]{1,0:T(8,128)S(1)}, f32[64,256]{1,0:T(8,128)S(1)}, u32[]{:S(2)}, u32[]{:S(2)}) collective-permute-start(f32[64,256]{1,0:T(8,128)S(1)} %get-tuple-element.20), channel_id=1, source_target_pairs={{0,3},{1,0},{2,1},{3,2},{4,7},{5,4},{6,5},{7,6},{8,11},{9,8},{10,9... | collective-permute-start | bytes 196616 | tf_op jit(solution)/shard_map/ppermute | solution.py:21
  13.8 1.2 fusion.160
  15.0 1.2 fusion.162
  18.9 1.4 bitcast_dynamic-update-slice_fusion
  20.9 1.5 collective-permute-start.1
  22.4 1.2 convolution_add_fusion.29
  23.7 1.2 fusion.152
  24.9 1.2 constant_dynamic-update-slice_fusion.3
  26.2 3.2 %collective-permute-start.14 = (f32[64,256]{1,0:T(8,128)S(1)}, f32[64,256]{1,0:T(8,128)S(1)}, u32[]{:S(2)}, u32[]{:S(2)}) collective-permute-start(f32[64,256]{1,0:T(8,128)S(1)} %bitcast.432), channel_id=1, source_target_pairs={{0,3},{1,0},{2,1},{3,2},{4,7},{5,4},{6,5},{7,6},{8,11},{9,8},{10,9... | collective-permute-start | bytes 196616 | tf_op jit(solution)/shard_map/ppermute | solution.py:21
  30.1 1.2 convolution_add_fusion.31
  31.6 1.2 fusion.154
  32.9 1.2 constant_dynamic-update-slice_fusion.15
  34.4 3.2 %collective-permute-start.8 = (f32[64,256]{1,0:T(8,128)S(1)}, f32[64,256]{1,0:T(8,128)S(1)}, u32[]{:S(2)}, u32[]{:S(2)}) collective-permute-start(f32[64,256]{1,0:T(8,128)S(1)} %bitcast.436), channel_id=1, source_target_pairs={{0,3},{1,0},{2,1},{3,2},{4,7},{5,4},{6,5},{7,6},{8,11},{9,8},{10,9... | collective-permute-start | bytes 196616 | tf_op jit(solution)/shard_map/ppermute | solution.py:21
  38.2 1.4 collective-permute-start.7
  40.5 3.0 %collective-permute-start.17 = (f32[64,256]{1,0:T(8,128)S(1)}, f32[64,256]{1,0:T(8,128)S(1)}, u32[]{:S(2)}, u32[]{:S(2)}) collective-permute-start(f32[64,256]{1,0:T(8,128)S(1)} %fusion.16), channel_id=1, source_target_pairs={{0,3},{1,0},{2,1},{3,2},{4,7},{5,4},{6,5},{7,6},{8,11},{9,8},{10,9... | collective-permute-start | bytes 196616 | tf_op jit(solution)/shard_map/ppermute | solution.py:21
  43.9 1.6 collective-permute-start.16
  46.8 2.2 %collective-permute-start.11 = (f32[64,256]{1,0:T(8,128)S(1)}, f32[64,256]{1,0:T(8,128)S(1)}, u32[]{:S(2)}, u32[]{:S(2)}) collective-permute-start(f32[64,256]{1,0:T(8,128)S(1)} %fusion.19), channel_id=1, source_target_pairs={{0,3},{1,0},{2,1},{3,2},{4,7},{5,4},{6,5},{7,6},{8,11},{9,8},{10,9... | collective-permute-start | bytes 196616 | tf_op jit(solution)/shard_map/ppermute | solution.py:21
  49.7 1.1 collective-permute-done.15
  50.7 1.7 collective-permute-start.10
  53.3 3.0 %collective-permute-start.26 = (f32[64,256]{1,0:T(8,128)S(1)}, f32[64,256]{1,0:T(8,128)S(1)}, u32[]{:S(2)}, u32[]{:S(2)}) collective-permute-start(f32[64,256]{1,0:T(8,128)S(1)} %get-tuple-element.52), channel_id=1, source_target_pairs={{0,3},{1,0},{2,1},{3,2},{4,7},{5,4},{6,5},{7,6},{8,11},{9,8},{10,9... | collective-permute-start | bytes 196616 | tf_op jit(solution)/shard_map/ppermute | solution.py:21
  56.6 1.4 collective-permute-start.25
  59.3 2.1 %collective-permute-start.20 = (f32[64,256]{1,0:T(8,128)S(1)}, f32[64,256]{1,0:T(8,128)S(1)}, u32[]{:S(2)}, u32[]{:S(2)}) collective-permute-start(f32[64,256]{1,0:T(8,128)S(1)} %get-tuple-element.46), channel_id=1, source_target_pairs={{0,3},{1,0},{2,1},{3,2},{4,7},{5,4},{6,5},{7,6},{8,11},{9,8},{10,9... | collective-permute-start | bytes 196616 | tf_op jit(solution)/shard_map/ppermute | solution.py:21
  62.3 1.1 collective-permute-done.24
  64.9 3.8 %collective-permute-start.29 = (f32[64,256]{1,0:T(8,128)S(1)}, f32[64,256]{1,0:T(8,128)S(1)}, u32[]{:S(2)}, u32[]{:S(2)}) collective-permute-start(f32[64,256]{1,0:T(8,128)S(1)} %fusion.10), channel_id=1, source_target_pairs={{0,3},{1,0},{2,1},{3,2},{4,7},{5,4},{6,5},{7,6},{8,11},{9,8},{10,9... | collective-permute-start | bytes 196616 | tf_op jit(solution)/shard_map/ppermute | solution.py:21
  70.8 3.0 %collective-permute-start.23 = (f32[64,256]{1,0:T(8,128)S(1)}, f32[64,256]{1,0:T(8,128)S(1)}, u32[]{:S(2)}, u32[]{:S(2)}) collective-permute-start(f32[64,256]{1,0:T(8,128)S(1)} %fusion.13), channel_id=1, source_target_pairs={{0,3},{1,0},{2,1},{3,2},{4,7},{5,4},{6,5},{7,6},{8,11},{9,8},{10,9... | collective-permute-start | bytes 196616 | tf_op jit(solution)/shard_map/ppermute | solution.py:21
  75.2 1.1 collective-permute-start.22
  77.3 3.4 %collective-permute-start.38 = (f32[64,256]{1,0:T(8,128)S(1)}, f32[64,256]{1,0:T(8,128)S(1)}, u32[]{:S(2)}, u32[]{:S(2)}) collective-permute-start(f32[64,256]{1,0:T(8,128)S(1)} %get-tuple-element.54), channel_id=1, source_target_pairs={{0,3},{1,0},{2,1},{3,2},{4,7},{5,4},{6,5},{7,6},{8,11},{9,8},{10,9... | collective-permute-start | bytes 196616 | tf_op jit(solution)/shard_map/ppermute | solution.py:21
  82.6 3.2 %collective-permute-start.32 = (f32[64,256]{1,0:T(8,128)S(1)}, f32[64,256]{1,0:T(8,128)S(1)}, u32[]{:S(2)}, u32[]{:S(2)}) collective-permute-start(f32[64,256]{1,0:T(8,128)S(1)} %get-tuple-element.48), channel_id=1, source_target_pairs={{0,3},{1,0},{2,1},{3,2},{4,7},{5,4},{6,5},{7,6},{8,11},{9,8},{10,9... | collective-permute-start | bytes 196616 | tf_op jit(solution)/shard_map/ppermute | solution.py:21
  87.1 1.2 collective-permute-start.31
  89.2 3.4 %collective-permute-start.41 = (f32[64,256]{1,0:T(8,128)S(1)}, f32[64,256]{1,0:T(8,128)S(1)}, u32[]{:S(2)}, u32[]{:S(2)}) collective-permute-start(f32[64,256]{1,0:T(8,128)S(1)} %fusion.4), channel_id=1, source_target_pairs={{0,3},{1,0},{2,1},{3,2},{4,7},{5,4},{6,5},{7,6},{8,11},{9,8},{10,9... | collective-permute-start | bytes 196616 | tf_op jit(solution)/shard_map/ppermute | solution.py:21
  93.0 1.3 collective-permute-start.40
  95.2 2.5 %collective-permute-start.35 = (f32[64,256]{1,0:T(8,128)S(1)}, f32[64,256]{1,0:T(8,128)S(1)}, u32[]{:S(2)}, u32[]{:S(2)}) collective-permute-start(f32[64,256]{1,0:T(8,128)S(1)} %fusion.7), channel_id=1, source_target_pairs={{0,3},{1,0},{2,1},{3,2},{4,7},{5,4},{6,5},{7,6},{8,11},{9,8},{10,9... | collective-permute-start | bytes 196616 | tf_op jit(solution)/shard_map/ppermute | solution.py:21
  101.8 1.5 collective-permute-start.34
  104.2 3.0 %collective-permute-start.47 = (f32[64,256]{1,0:T(8,128)S(1)}, f32[64,256]{1,0:T(8,128)S(1)}, u32[]{:S(2)}, u32[]{:S(2)}) collective-permute-start(f32[64,256]{1,0:T(8,128)S(1)} %fusion.2), channel_id=1, source_target_pairs={{0,3},{1,0},{2,1},{3,2},{4,7},{5,4},{6,5},{7,6},{8,11},{9,8},{10,9... | collective-permute-start | bytes 196616 | tf_op jit(solution)/shard_map/ppermute | solution.py:21
  107.2 0.9 collective-permute-start.46
  109.3 3.0 %collective-permute-start.44 = (f32[64,256]{1,0:T(8,128)S(1)}, f32[64,256]{1,0:T(8,128)S(1)}, u32[]{:S(2)}, u32[]{:S(2)}) collective-permute-start(f32[64,256]{1,0:T(8,128)S(1)} %fusion.5), channel_id=1, source_target_pairs={{0,3},{1,0},{2,1},{3,2},{4,7},{5,4},{6,5},{7,6},{8,11},{9,8},{10,9... | collective-permute-start | bytes 196616 | tf_op jit(solution)/shard_map/ppermute | solution.py:21
  113.3 1.5 collective-permute-start.43
  115.8 3.1 %collective-permute-done.42 = f32[64,256]{1,0:T(8,128)S(1)} collective-permute-done((f32[64,256]{1,0:T(8,128)S(1)}, f32[64,256]{1,0:T(8,128)S(1)}, u32[]{:S(2)}, u32[]{:S(2)}) %collective-permute-start.42) | collective-permute-done | bytes 65568 | tf_op jit(solution)/shard_map/ppermute | solution.py:21
  121.4 2.6 %collective-permute-start.51 = (f32[2,16,512]{2,1,0:T(8,128)S(1)}, f32[2,16,512]{2,1,0:T(8,128)S(1)}, u32[]{:S(2)}, u32[]{:S(2)}) collective-permute-start(f32[2,16,512]{2,1,0:T(8,128)S(1)} %get-tuple-element.25), channel_id=1, source_target_pairs={{0,24},{4,28},{8,16},{12,20},{16,8},{20,12},{24,0},{28,4},{1,25},{... | collective-permute-start | bytes 196616 | tf_op jit(solution)/shard_map/ppermute | solution.py:64
  125.6 1.2 collective-permute-done.51
  126.9 1.4 collective-permute-done.50
  130.0 1.0 reshape.397
  131.8 1.0 convolution_bitcast_fusion
  132.8 1.0 reshape.398
  133.8 1.1 copy_subtract_fusion
  134.9 2.2 %collective-permute-start.54 = (f32[16,1280]{1,0:T(8,128)S(1)}, f32[16,1280]{1,0:T(8,128)S(1)}, u32[]{:S(2)}, u32[]{:S(2)}) collective-permute-start(f32[16,1280]{1,0:T(8,128)S(1)} %get-tuple-element.36), channel_id=1, source_target_pairs={{0,3},{1,0},{2,1},{3,2},{4,7},{5,4},{6,5},{7,6},{8,11},{9,8},{10,9... | collective-permute-start | bytes 245768 | tf_op jit(solution)/shard_map/ppermute | solution.py:21
  137.8 2.1 %collective-permute-done.54 = f32[16,1280]{1,0:T(8,128)S(1)} collective-permute-done((f32[16,1280]{1,0:T(8,128)S(1)}, f32[16,1280]{1,0:T(8,128)S(1)}, u32[]{:S(2)}, u32[]{:S(2)}) %collective-permute-start.54) | collective-permute-done | bytes 81952 | tf_op jit(solution)/shard_map/ppermute | solution.py:21
  139.9 5.1 %collective-permute-done.53 = f32[16,1280]{1,0:T(8,128)S(1)} collective-permute-done((f32[16,1280]{1,0:T(8,128)S(1)}, f32[16,1280]{1,0:T(8,128)S(1)}, u32[]{:S(2)}, u32[]{:S(2)}) %collective-permute-start.53) | collective-permute-done | bytes 81952 | tf_op jit(solution)/shard_map/ppermute | solution.py:21
  145.0 1.7 %fusion.26 = f32[16,256]{1,0:T(8,128)S(1)} fusion(f32[2,256,1024]{2,1,0:T(8,128)} %param.20, f32[16,1280]{1,0:T(8,128)S(1)} %fusion.231), kind=kOutput, calls=%fused_computation.62 | convolution fusion | flops 25165824 | bytes 1130496 | tf_op jit(solution)/shard_map/dot_general | solution.py:10
  146.8 1.0 collective-permute-start.57
  147.7 1.1 collective-permute-start.55
  148.8 1.0 collective-permute-start.56
  150.0 3.3 %collective-permute-done.55 = f32[16,256]{1,0:T(8,128)S(1)} collective-permute-done((f32[16,256]{1,0:T(8,128)S(1)}, f32[16,256]{1,0:T(8,128)S(1)}, u32[]{:S(2)}, u32[]{:S(2)}) %collective-permute-start.55) | collective-permute-done | bytes 16416 | tf_op jit(solution)/shard_map/ppermute | solution.py:21
  154.0 2.5 %collective-permute-start.60 = (f32[16,256]{1,0:T(8,128)S(1)}, f32[16,256]{1,0:T(8,128)S(1)}, u32[]{:S(2)}, u32[]{:S(2)}) collective-permute-start(f32[16,256]{1,0:T(8,128)S(1)} %slice_subtract_fusion), channel_id=1, source_target_pairs={{0,3},{1,0},{2,1},{3,2},{4,7},{5,4},{6,5},{7,6},{8,11},{9,8},{10,9... | collective-permute-start | bytes 49160 | tf_op jit(solution)/shard_map/ppermute | solution.py:21
  157.4 2.0 %copy.32 = f32[1,4,256,128]{3,2,1,0:T(8,128)} copy(f32[1,4,256,128]{2,3,1,0:T(8,128)} %maximum_bitcast_fusion) | data formatting | bytes 1048576
  160.0 1.1 fusion.67
  161.1 2.9 %collective-permute-done.59 = f32[16,256]{1,0:T(8,128)S(1)} collective-permute-done((f32[16,256]{1,0:T(8,128)S(1)}, f32[16,256]{1,0:T(8,128)S(1)}, u32[]{:S(2)}, u32[]{:S(2)}) %collective-permute-start.59) | collective-permute-done | bytes 16416 | tf_op jit(solution)/shard_map/ppermute | solution.py:21
  164.0 1.1 fusion.69
  165.2 1.1 fusion.71
  166.4 1.2 fusion.24
  (221 shorter events, 40.8 us)
Async XLA Ops:
  0.6 30.7 %copy-start = (f32[1,3,256,1024]{3,2,1,0:T(8,128)S(1)}, f32[1,3,256,1024]{3,2,1,0:T(8,128)}, u32[]{:S(2)}) copy-start(f32[1,3,256,1024]{3,2,1,0:T(8,128)} %param.14) | copy-start | bytes 9437188
  4.3 19.3 %collective-permute-start.5 = (f32[64,256]{1,0:T(8,128)}, f32[64,256]{1,0:T(8,128)}, u32[]{:S(2)}, u32[]{:S(2)}) collective-permute-start(f32[64,256]{1,0:T(8,128)} %get-tuple-element.21), channel_id=1, source_target_pairs={{0,3},{1,0},{2,1},{3,2},{4,7},{5,4},{6,5},{7,6},{8,11},{9,8},{10,9... | collective-permute-start | bytes 196616 | tf_op jit(solution)/shard_map/ppermute | solution.py:21
  9.4 11.5 %collective-permute-start.3 = (f32[64,256]{1,0:T(8,128)}, f32[64,256]{1,0:T(8,128)}, u32[]{:S(2)}, u32[]{:S(2)}) collective-permute-start(f32[64,256]{1,0:T(8,128)} %get-tuple-element.21), channel_id=1, source_target_pairs={{0,1},{1,2},{2,3},{3,0},{4,5},{5,6},{6,7},{7,4},{8,9},{9,10},{10,1... | collective-permute-start | bytes 196616 | tf_op jit(solution)/shard_map/ppermute | solution.py:21
  9.4 15.5 %collective-permute-start.4 = (f32[64,256]{1,0:T(8,128)}, f32[64,256]{1,0:T(8,128)S(1)}, u32[]{:S(2)}, u32[]{:S(2)}) collective-permute-start(f32[64,256]{1,0:T(8,128)} %get-tuple-element.21), channel_id=1, source_target_pairs={{0,2},{1,3},{2,0},{3,1},{4,6},{5,7},{6,4},{7,5},{8,10},{9,11},{10,... | collective-permute-start | bytes 196616 | tf_op jit(solution)/shard_map/ppermute | solution.py:21
  10.4 21.2 %collective-permute-start.2 = (f32[64,256]{1,0:T(8,128)S(1)}, f32[64,256]{1,0:T(8,128)S(1)}, u32[]{:S(2)}, u32[]{:S(2)}) collective-permute-start(f32[64,256]{1,0:T(8,128)S(1)} %get-tuple-element.20), channel_id=1, source_target_pairs={{0,3},{1,0},{2,1},{3,2},{4,7},{5,4},{6,5},{7,6},{8,11},{9,8},{10,9... | collective-permute-start | bytes 196616 | tf_op jit(solution)/shard_map/ppermute | solution.py:21
  13.2 16.2 %collective-permute-start = (f32[64,256]{1,0:T(8,128)S(1)}, f32[64,256]{1,0:T(8,128)S(1)}, u32[]{:S(2)}, u32[]{:S(2)}) collective-permute-start(f32[64,256]{1,0:T(8,128)S(1)} %get-tuple-element.20), channel_id=1, source_target_pairs={{0,1},{1,2},{2,3},{3,0},{4,5},{5,6},{6,7},{7,4},{8,9},{9,10},{10,1... | collective-permute-start | bytes 196616 | tf_op jit(solution)/shard_map/ppermute | solution.py:21
  20.9 11.9 %collective-permute-start.1 = (f32[64,256]{1,0:T(8,128)S(1)}, f32[64,256]{1,0:T(8,128)S(1)}, u32[]{:S(2)}, u32[]{:S(2)}) collective-permute-start(f32[64,256]{1,0:T(8,128)S(1)} %get-tuple-element.20), channel_id=1, source_target_pairs={{0,2},{1,3},{2,0},{3,1},{4,6},{5,7},{6,4},{7,5},{8,10},{9,11},{10,... | collective-permute-start | bytes 196616 | tf_op jit(solution)/shard_map/ppermute | solution.py:21
  26.2 13.7 %collective-permute-start.14 = (f32[64,256]{1,0:T(8,128)S(1)}, f32[64,256]{1,0:T(8,128)S(1)}, u32[]{:S(2)}, u32[]{:S(2)}) collective-permute-start(f32[64,256]{1,0:T(8,128)S(1)} %bitcast.432), channel_id=1, source_target_pairs={{0,3},{1,0},{2,1},{3,2},{4,7},{5,4},{6,5},{7,6},{8,11},{9,8},{10,9... | collective-permute-start | bytes 196616 | tf_op jit(solution)/shard_map/ppermute | solution.py:21
  29.4 8.9 %collective-permute-start.12 = (f32[64,256]{1,0:T(8,128)S(1)}, f32[64,256]{1,0:T(8,128)S(1)}, u32[]{:S(2)}, u32[]{:S(2)}) collective-permute-start(f32[64,256]{1,0:T(8,128)S(1)} %bitcast.433), channel_id=1, source_target_pairs={{0,1},{1,2},{2,3},{3,0},{4,5},{5,6},{6,7},{7,4},{8,9},{9,10},{10,1... | collective-permute-start | bytes 196616 | tf_op jit(solution)/shard_map/ppermute | solution.py:21
  29.4 10.8 %collective-permute-start.13 = (f32[64,256]{1,0:T(8,128)S(1)}, f32[64,256]{1,0:T(8,128)S(1)}, u32[]{:S(2)}, u32[]{:S(2)}) collective-permute-start(f32[64,256]{1,0:T(8,128)S(1)} %bitcast.434), channel_id=1, source_target_pairs={{0,2},{1,3},{2,0},{3,1},{4,6},{5,7},{6,4},{7,5},{8,10},{9,11},{10,... | collective-permute-start | bytes 196616 | tf_op jit(solution)/shard_map/ppermute | solution.py:21
  34.4 11.4 %collective-permute-start.8 = (f32[64,256]{1,0:T(8,128)S(1)}, f32[64,256]{1,0:T(8,128)S(1)}, u32[]{:S(2)}, u32[]{:S(2)}) collective-permute-start(f32[64,256]{1,0:T(8,128)S(1)} %bitcast.436), channel_id=1, source_target_pairs={{0,3},{1,0},{2,1},{3,2},{4,7},{5,4},{6,5},{7,6},{8,11},{9,8},{10,9... | collective-permute-start | bytes 196616 | tf_op jit(solution)/shard_map/ppermute | solution.py:21
  37.6 6.3 %collective-permute-start.6 = (f32[64,256]{1,0:T(8,128)S(1)}, f32[64,256]{1,0:T(8,128)S(1)}, u32[]{:S(2)}, u32[]{:S(2)}) collective-permute-start(f32[64,256]{1,0:T(8,128)S(1)} %bitcast.437), channel_id=1, source_target_pairs={{0,1},{1,2},{2,3},{3,0},{4,5},{5,6},{6,7},{7,4},{8,9},{9,10},{10,1... | collective-permute-start | bytes 196616 | tf_op jit(solution)/shard_map/ppermute | solution.py:21
  38.2 8.2 %collective-permute-start.7 = (f32[64,256]{1,0:T(8,128)S(1)}, f32[64,256]{1,0:T(8,128)S(1)}, u32[]{:S(2)}, u32[]{:S(2)}) collective-permute-start(f32[64,256]{1,0:T(8,128)S(1)} %bitcast.438), channel_id=1, source_target_pairs={{0,2},{1,3},{2,0},{3,1},{4,6},{5,7},{6,4},{7,5},{8,10},{9,11},{10,... | collective-permute-start | bytes 196616 | tf_op jit(solution)/shard_map/ppermute | solution.py:21
  40.5 12.1 %collective-permute-start.17 = (f32[64,256]{1,0:T(8,128)S(1)}, f32[64,256]{1,0:T(8,128)S(1)}, u32[]{:S(2)}, u32[]{:S(2)}) collective-permute-start(f32[64,256]{1,0:T(8,128)S(1)} %fusion.16), channel_id=1, source_target_pairs={{0,3},{1,0},{2,1},{3,2},{4,7},{5,4},{6,5},{7,6},{8,11},{9,8},{10,9... | collective-permute-start | bytes 196616 | tf_op jit(solution)/shard_map/ppermute | solution.py:21
  43.8 6.9 %collective-permute-start.15 = (f32[64,256]{1,0:T(8,128)S(1)}, f32[64,256]{1,0:T(8,128)S(1)}, u32[]{:S(2)}, u32[]{:S(2)}) collective-permute-start(f32[64,256]{1,0:T(8,128)S(1)} %fusion.16), channel_id=1, source_target_pairs={{0,1},{1,2},{2,3},{3,0},{4,5},{5,6},{6,7},{7,4},{8,9},{9,10},{10,1... | collective-permute-start | bytes 196616 | tf_op jit(solution)/shard_map/ppermute | solution.py:21
  43.9 9.1 %collective-permute-start.16 = (f32[64,256]{1,0:T(8,128)S(1)}, f32[64,256]{1,0:T(8,128)S(1)}, u32[]{:S(2)}, u32[]{:S(2)}) collective-permute-start(f32[64,256]{1,0:T(8,128)S(1)} %fusion.16), channel_id=1, source_target_pairs={{0,2},{1,3},{2,0},{3,1},{4,6},{5,7},{6,4},{7,5},{8,10},{9,11},{10,... | collective-permute-start | bytes 196616 | tf_op jit(solution)/shard_map/ppermute | solution.py:21
  46.8 11.6 %collective-permute-start.11 = (f32[64,256]{1,0:T(8,128)S(1)}, f32[64,256]{1,0:T(8,128)S(1)}, u32[]{:S(2)}, u32[]{:S(2)}) collective-permute-start(f32[64,256]{1,0:T(8,128)S(1)} %fusion.19), channel_id=1, source_target_pairs={{0,3},{1,0},{2,1},{3,2},{4,7},{5,4},{6,5},{7,6},{8,11},{9,8},{10,9... | collective-permute-start | bytes 196616 | tf_op jit(solution)/shard_map/ppermute | solution.py:21
  49.2 7.4 %collective-permute-start.9 = (f32[64,256]{1,0:T(8,128)S(1)}, f32[64,256]{1,0:T(8,128)S(1)}, u32[]{:S(2)}, u32[]{:S(2)}) collective-permute-start(f32[64,256]{1,0:T(8,128)S(1)} %fusion.19), channel_id=1, source_target_pairs={{0,1},{1,2},{2,3},{3,0},{4,5},{5,6},{6,7},{7,4},{8,9},{9,10},{10,1... | collective-permute-start | bytes 196616 | tf_op jit(solution)/shard_map/ppermute | solution.py:21
  50.7 8.2 %collective-permute-start.10 = (f32[64,256]{1,0:T(8,128)S(1)}, f32[64,256]{1,0:T(8,128)S(1)}, u32[]{:S(2)}, u32[]{:S(2)}) collective-permute-start(f32[64,256]{1,0:T(8,128)S(1)} %fusion.19), channel_id=1, source_target_pairs={{0,2},{1,3},{2,0},{3,1},{4,6},{5,7},{6,4},{7,5},{8,10},{9,11},{10,... | collective-permute-start | bytes 196616 | tf_op jit(solution)/shard_map/ppermute | solution.py:21
  53.3 11.0 %collective-permute-start.26 = (f32[64,256]{1,0:T(8,128)S(1)}, f32[64,256]{1,0:T(8,128)S(1)}, u32[]{:S(2)}, u32[]{:S(2)}) collective-permute-start(f32[64,256]{1,0:T(8,128)S(1)} %get-tuple-element.52), channel_id=1, source_target_pairs={{0,3},{1,0},{2,1},{3,2},{4,7},{5,4},{6,5},{7,6},{8,11},{9,8},{10,9... | collective-permute-start | bytes 196616 | tf_op jit(solution)/shard_map/ppermute | solution.py:21
  56.5 6.9 %collective-permute-start.24 = (f32[64,256]{1,0:T(8,128)S(1)}, f32[64,256]{1,0:T(8,128)S(1)}, u32[]{:S(2)}, u32[]{:S(2)}) collective-permute-start(f32[64,256]{1,0:T(8,128)S(1)} %get-tuple-element.52), channel_id=1, source_target_pairs={{0,1},{1,2},{2,3},{3,0},{4,5},{5,6},{6,7},{7,4},{8,9},{9,10},{10,1... | collective-permute-start | bytes 196616 | tf_op jit(solution)/shard_map/ppermute | solution.py:21
  56.6 8.0 %collective-permute-start.25 = (f32[64,256]{1,0:T(8,128)S(1)}, f32[64,256]{1,0:T(8,128)S(1)}, u32[]{:S(2)}, u32[]{:S(2)}) collective-permute-start(f32[64,256]{1,0:T(8,128)S(1)} %get-tuple-element.52), channel_id=1, source_target_pairs={{0,2},{1,3},{2,0},{3,1},{4,6},{5,7},{6,4},{7,5},{8,10},{9,11},{10,... | collective-permute-start | bytes 196616 | tf_op jit(solution)/shard_map/ppermute | solution.py:21
  59.3 10.7 %collective-permute-start.20 = (f32[64,256]{1,0:T(8,128)S(1)}, f32[64,256]{1,0:T(8,128)S(1)}, u32[]{:S(2)}, u32[]{:S(2)}) collective-permute-start(f32[64,256]{1,0:T(8,128)S(1)} %get-tuple-element.46), channel_id=1, source_target_pairs={{0,3},{1,0},{2,1},{3,2},{4,7},{5,4},{6,5},{7,6},{8,11},{9,8},{10,9... | collective-permute-start | bytes 196616 | tf_op jit(solution)/shard_map/ppermute | solution.py:21
  61.7 7.3 %collective-permute-start.18 = (f32[64,256]{1,0:T(8,128)S(1)}, f32[64,256]{1,0:T(8,128)S(1)}, u32[]{:S(2)}, u32[]{:S(2)}) collective-permute-start(f32[64,256]{1,0:T(8,128)S(1)} %get-tuple-element.46), channel_id=1, source_target_pairs={{0,1},{1,2},{2,3},{3,0},{4,5},{5,6},{6,7},{7,4},{8,9},{9,10},{10,1... | collective-permute-start | bytes 196616 | tf_op jit(solution)/shard_map/ppermute | solution.py:21
  63.4 7.1 %collective-permute-start.19 = (f32[64,256]{1,0:T(8,128)S(1)}, f32[64,256]{1,0:T(8,128)S(1)}, u32[]{:S(2)}, u32[]{:S(2)}) collective-permute-start(f32[64,256]{1,0:T(8,128)S(1)} %get-tuple-element.46), channel_id=1, source_target_pairs={{0,2},{1,3},{2,0},{3,1},{4,6},{5,7},{6,4},{7,5},{8,10},{9,11},{10,... | collective-permute-start | bytes 196616 | tf_op jit(solution)/shard_map/ppermute | solution.py:21
  64.9 11.7 %collective-permute-start.29 = (f32[64,256]{1,0:T(8,128)S(1)}, f32[64,256]{1,0:T(8,128)S(1)}, u32[]{:S(2)}, u32[]{:S(2)}) collective-permute-start(f32[64,256]{1,0:T(8,128)S(1)} %fusion.10), channel_id=1, source_target_pairs={{0,3},{1,0},{2,1},{3,2},{4,7},{5,4},{6,5},{7,6},{8,11},{9,8},{10,9... | collective-permute-start | bytes 196616 | tf_op jit(solution)/shard_map/ppermute | solution.py:21
  68.9 6.3 %collective-permute-start.27 = (f32[64,256]{1,0:T(8,128)S(1)}, f32[64,256]{1,0:T(8,128)S(1)}, u32[]{:S(2)}, u32[]{:S(2)}) collective-permute-start(f32[64,256]{1,0:T(8,128)S(1)} %fusion.10), channel_id=1, source_target_pairs={{0,1},{1,2},{2,3},{3,0},{4,5},{5,6},{6,7},{7,4},{8,9},{9,10},{10,1... | collective-permute-start | bytes 196616 | tf_op jit(solution)/shard_map/ppermute | solution.py:21
  69.0 7.9 %collective-permute-start.28 = (f32[64,256]{1,0:T(8,128)S(1)}, f32[64,256]{1,0:T(8,128)S(1)}, u32[]{:S(2)}, u32[]{:S(2)}) collective-permute-start(f32[64,256]{1,0:T(8,128)S(1)} %fusion.10), channel_id=1, source_target_pairs={{0,2},{1,3},{2,0},{3,1},{4,6},{5,7},{6,4},{7,5},{8,10},{9,11},{10,... | collective-permute-start | bytes 196616 | tf_op jit(solution)/shard_map/ppermute | solution.py:21
  70.8 11.1 %collective-permute-start.23 = (f32[64,256]{1,0:T(8,128)S(1)}, f32[64,256]{1,0:T(8,128)S(1)}, u32[]{:S(2)}, u32[]{:S(2)}) collective-permute-start(f32[64,256]{1,0:T(8,128)S(1)} %fusion.13), channel_id=1, source_target_pairs={{0,3},{1,0},{2,1},{3,2},{4,7},{5,4},{6,5},{7,6},{8,11},{9,8},{10,9... | collective-permute-start | bytes 196616 | tf_op jit(solution)/shard_map/ppermute | solution.py:21
  74.0 7.0 %collective-permute-start.21 = (f32[64,256]{1,0:T(8,128)S(1)}, f32[64,256]{1,0:T(8,128)S(1)}, u32[]{:S(2)}, u32[]{:S(2)}) collective-permute-start(f32[64,256]{1,0:T(8,128)S(1)} %fusion.13), channel_id=1, source_target_pairs={{0,1},{1,2},{2,3},{3,0},{4,5},{5,6},{6,7},{7,4},{8,9},{9,10},{10,1... | collective-permute-start | bytes 196616 | tf_op jit(solution)/shard_map/ppermute | solution.py:21
  75.2 7.1 %collective-permute-start.22 = (f32[64,256]{1,0:T(8,128)S(1)}, f32[64,256]{1,0:T(8,128)S(1)}, u32[]{:S(2)}, u32[]{:S(2)}) collective-permute-start(f32[64,256]{1,0:T(8,128)S(1)} %fusion.13), channel_id=1, source_target_pairs={{0,2},{1,3},{2,0},{3,1},{4,6},{5,7},{6,4},{7,5},{8,10},{9,11},{10,... | collective-permute-start | bytes 196616 | tf_op jit(solution)/shard_map/ppermute | solution.py:21
  77.3 11.3 %collective-permute-start.38 = (f32[64,256]{1,0:T(8,128)S(1)}, f32[64,256]{1,0:T(8,128)S(1)}, u32[]{:S(2)}, u32[]{:S(2)}) collective-permute-start(f32[64,256]{1,0:T(8,128)S(1)} %get-tuple-element.54), channel_id=1, source_target_pairs={{0,3},{1,0},{2,1},{3,2},{4,7},{5,4},{6,5},{7,6},{8,11},{9,8},{10,9... | collective-permute-start | bytes 196616 | tf_op jit(solution)/shard_map/ppermute | solution.py:21
  81.0 6.1 %collective-permute-start.36 = (f32[64,256]{1,0:T(8,128)S(1)}, f32[64,256]{1,0:T(8,128)S(1)}, u32[]{:S(2)}, u32[]{:S(2)}) collective-permute-start(f32[64,256]{1,0:T(8,128)S(1)} %get-tuple-element.54), channel_id=1, source_target_pairs={{0,1},{1,2},{2,3},{3,0},{4,5},{5,6},{6,7},{7,4},{8,9},{9,10},{10,1... | collective-permute-start | bytes 196616 | tf_op jit(solution)/shard_map/ppermute | solution.py:21
  81.0 7.8 %collective-permute-start.37 = (f32[64,256]{1,0:T(8,128)S(1)}, f32[64,256]{1,0:T(8,128)S(1)}, u32[]{:S(2)}, u32[]{:S(2)}) collective-permute-start(f32[64,256]{1,0:T(8,128)S(1)} %get-tuple-element.54), channel_id=1, source_target_pairs={{0,2},{1,3},{2,0},{3,1},{4,6},{5,7},{6,4},{7,5},{8,10},{9,11},{10,... | collective-permute-start | bytes 196616 | tf_op jit(solution)/shard_map/ppermute | solution.py:21
  82.6 12.0 %collective-permute-start.32 = (f32[64,256]{1,0:T(8,128)S(1)}, f32[64,256]{1,0:T(8,128)S(1)}, u32[]{:S(2)}, u32[]{:S(2)}) collective-permute-start(f32[64,256]{1,0:T(8,128)S(1)} %get-tuple-element.48), channel_id=1, source_target_pairs={{0,3},{1,0},{2,1},{3,2},{4,7},{5,4},{6,5},{7,6},{8,11},{9,8},{10,9... | collective-permute-start | bytes 196616 | tf_op jit(solution)/shard_map/ppermute | solution.py:21
  86.1 6.9 %collective-permute-start.30 = (f32[64,256]{1,0:T(8,128)S(1)}, f32[64,256]{1,0:T(8,128)S(1)}, u32[]{:S(2)}, u32[]{:S(2)}) collective-permute-start(f32[64,256]{1,0:T(8,128)S(1)} %get-tuple-element.48), channel_id=1, source_target_pairs={{0,1},{1,2},{2,3},{3,0},{4,5},{5,6},{6,7},{7,4},{8,9},{9,10},{10,1... | collective-permute-start | bytes 196616 | tf_op jit(solution)/shard_map/ppermute | solution.py:21
  87.1 7.8 %collective-permute-start.31 = (f32[64,256]{1,0:T(8,128)S(1)}, f32[64,256]{1,0:T(8,128)S(1)}, u32[]{:S(2)}, u32[]{:S(2)}) collective-permute-start(f32[64,256]{1,0:T(8,128)S(1)} %get-tuple-element.48), channel_id=1, source_target_pairs={{0,2},{1,3},{2,0},{3,1},{4,6},{5,7},{6,4},{7,5},{8,10},{9,11},{10,... | collective-permute-start | bytes 196616 | tf_op jit(solution)/shard_map/ppermute | solution.py:21
  89.2 14.4 %collective-permute-start.41 = (f32[64,256]{1,0:T(8,128)S(1)}, f32[64,256]{1,0:T(8,128)S(1)}, u32[]{:S(2)}, u32[]{:S(2)}) collective-permute-start(f32[64,256]{1,0:T(8,128)S(1)} %fusion.4), channel_id=1, source_target_pairs={{0,3},{1,0},{2,1},{3,2},{4,7},{5,4},{6,5},{7,6},{8,11},{9,8},{10,9... | collective-permute-start | bytes 196616 | tf_op jit(solution)/shard_map/ppermute | solution.py:21
  92.9 8.9 %collective-permute-start.39 = (f32[64,256]{1,0:T(8,128)S(1)}, f32[64,256]{1,0:T(8,128)S(1)}, u32[]{:S(2)}, u32[]{:S(2)}) collective-permute-start(f32[64,256]{1,0:T(8,128)S(1)} %fusion.4), channel_id=1, source_target_pairs={{0,1},{1,2},{2,3},{3,0},{4,5},{5,6},{6,7},{7,4},{8,9},{9,10},{10,1... | collective-permute-start | bytes 196616 | tf_op jit(solution)/shard_map/ppermute | solution.py:21
  93.0 11.0 %collective-permute-start.40 = (f32[64,256]{1,0:T(8,128)S(1)}, f32[64,256]{1,0:T(8,128)S(1)}, u32[]{:S(2)}, u32[]{:S(2)}) collective-permute-start(f32[64,256]{1,0:T(8,128)S(1)} %fusion.4), channel_id=1, source_target_pairs={{0,2},{1,3},{2,0},{3,1},{4,6},{5,7},{6,4},{7,5},{8,10},{9,11},{10,... | collective-permute-start | bytes 196616 | tf_op jit(solution)/shard_map/ppermute | solution.py:21
  95.2 13.5 %collective-permute-start.35 = (f32[64,256]{1,0:T(8,128)S(1)}, f32[64,256]{1,0:T(8,128)S(1)}, u32[]{:S(2)}, u32[]{:S(2)}) collective-permute-start(f32[64,256]{1,0:T(8,128)S(1)} %fusion.7), channel_id=1, source_target_pairs={{0,3},{1,0},{2,1},{3,2},{4,7},{5,4},{6,5},{7,6},{8,11},{9,8},{10,9... | collective-permute-start | bytes 196616 | tf_op jit(solution)/shard_map/ppermute | solution.py:21
  98.0 9.2 %collective-permute-start.33 = (f32[64,256]{1,0:T(8,128)S(1)}, f32[64,256]{1,0:T(8,128)S(1)}, u32[]{:S(2)}, u32[]{:S(2)}) collective-permute-start(f32[64,256]{1,0:T(8,128)S(1)} %fusion.7), channel_id=1, source_target_pairs={{0,1},{1,2},{2,3},{3,0},{4,5},{5,6},{6,7},{7,4},{8,9},{9,10},{10,1... | collective-permute-start | bytes 196616 | tf_op jit(solution)/shard_map/ppermute | solution.py:21
  101.8 7.2 %collective-permute-start.34 = (f32[64,256]{1,0:T(8,128)S(1)}, f32[64,256]{1,0:T(8,128)S(1)}, u32[]{:S(2)}, u32[]{:S(2)}) collective-permute-start(f32[64,256]{1,0:T(8,128)S(1)} %fusion.7), channel_id=1, source_target_pairs={{0,2},{1,3},{2,0},{3,1},{4,6},{5,7},{6,4},{7,5},{8,10},{9,11},{10,... | collective-permute-start | bytes 196616 | tf_op jit(solution)/shard_map/ppermute | solution.py:21
  104.2 10.9 %collective-permute-start.47 = (f32[64,256]{1,0:T(8,128)S(1)}, f32[64,256]{1,0:T(8,128)S(1)}, u32[]{:S(2)}, u32[]{:S(2)}) collective-permute-start(f32[64,256]{1,0:T(8,128)S(1)} %fusion.2), channel_id=1, source_target_pairs={{0,3},{1,0},{2,1},{3,2},{4,7},{5,4},{6,5},{7,6},{8,11},{9,8},{10,9... | collective-permute-start | bytes 196616 | tf_op jit(solution)/shard_map/ppermute | solution.py:21
  107.2 6.1 %collective-permute-start.45 = (f32[64,256]{1,0:T(8,128)S(1)}, f32[64,256]{1,0:T(8,128)S(1)}, u32[]{:S(2)}, u32[]{:S(2)}) collective-permute-start(f32[64,256]{1,0:T(8,128)S(1)} %fusion.2), channel_id=1, source_target_pairs={{0,1},{1,2},{2,3},{3,0},{4,5},{5,6},{6,7},{7,4},{8,9},{9,10},{10,1... | collective-permute-start | bytes 196616 | tf_op jit(solution)/shard_map/ppermute | solution.py:21
  107.2 8.2 %collective-permute-start.46 = (f32[64,256]{1,0:T(8,128)S(1)}, f32[64,256]{1,0:T(8,128)S(1)}, u32[]{:S(2)}, u32[]{:S(2)}) collective-permute-start(f32[64,256]{1,0:T(8,128)S(1)} %fusion.2), channel_id=1, source_target_pairs={{0,2},{1,3},{2,0},{3,1},{4,6},{5,7},{6,4},{7,5},{8,10},{9,11},{10,... | collective-permute-start | bytes 196616 | tf_op jit(solution)/shard_map/ppermute | solution.py:21
  109.3 9.8 %collective-permute-start.44 = (f32[64,256]{1,0:T(8,128)S(1)}, f32[64,256]{1,0:T(8,128)S(1)}, u32[]{:S(2)}, u32[]{:S(2)}) collective-permute-start(f32[64,256]{1,0:T(8,128)S(1)} %fusion.5), channel_id=1, source_target_pairs={{0,3},{1,0},{2,1},{3,2},{4,7},{5,4},{6,5},{7,6},{8,11},{9,8},{10,9... | collective-permute-start | bytes 196616 | tf_op jit(solution)/shard_map/ppermute | solution.py:21
  112.6 6.2 %collective-permute-start.42 = (f32[64,256]{1,0:T(8,128)S(1)}, f32[64,256]{1,0:T(8,128)S(1)}, u32[]{:S(2)}, u32[]{:S(2)}) collective-permute-start(f32[64,256]{1,0:T(8,128)S(1)} %fusion.5), channel_id=1, source_target_pairs={{0,1},{1,2},{2,3},{3,0},{4,5},{5,6},{6,7},{7,4},{8,9},{9,10},{10,1... | collective-permute-start | bytes 196616 | tf_op jit(solution)/shard_map/ppermute | solution.py:21
  113.3 6.2 %collective-permute-start.43 = (f32[64,256]{1,0:T(8,128)S(1)}, f32[64,256]{1,0:T(8,128)S(1)}, u32[]{:S(2)}, u32[]{:S(2)}) collective-permute-start(f32[64,256]{1,0:T(8,128)S(1)} %fusion.5), channel_id=1, source_target_pairs={{0,2},{1,3},{2,0},{3,1},{4,6},{5,7},{6,4},{7,5},{8,10},{9,11},{10,... | collective-permute-start | bytes 196616 | tf_op jit(solution)/shard_map/ppermute | solution.py:21
  120.0 1.4 collective-permute-start.48
  121.4 5.4 %collective-permute-start.51 = (f32[2,16,512]{2,1,0:T(8,128)S(1)}, f32[2,16,512]{2,1,0:T(8,128)S(1)}, u32[]{:S(2)}, u32[]{:S(2)}) collective-permute-start(f32[2,16,512]{2,1,0:T(8,128)S(1)} %get-tuple-element.25), channel_id=1, source_target_pairs={{0,24},{4,28},{8,16},{12,20},{16,8},{20,12},{24,0},{28,4},{1,25},{... | collective-permute-start | bytes 196616 | tf_op jit(solution)/shard_map/ppermute | solution.py:64
  124.0 4.3 %collective-permute-start.50 = (f32[2,16,512]{2,1,0:T(8,128)S(1)}, f32[2,16,512]{2,1,0:T(8,128)S(1)}, u32[]{:S(2)}, u32[]{:S(2)}) collective-permute-start(f32[2,16,512]{2,1,0:T(8,128)S(1)} %get-tuple-element.24), channel_id=1, source_target_pairs={{0,16},{4,20},{8,24},{12,28},{16,0},{20,4},{24,8},{28,12},{1,17},{... | collective-permute-start | bytes 196616 | tf_op jit(solution)/shard_map/ppermute | solution.py:64
  124.4 4.3 %collective-permute-start.49 = (f32[2,16,512]{2,1,0:T(8,128)S(1)}, f32[2,16,512]{2,1,0:T(8,128)S(1)}, u32[]{:S(2)}, u32[]{:S(2)}) collective-permute-start(f32[2,16,512]{2,1,0:T(8,128)S(1)} %get-tuple-element.23), channel_id=1, source_target_pairs={{0,8},{4,12},{8,0},{12,4},{16,24},{20,28},{24,16},{28,20},{1,9},{5... | collective-permute-start | bytes 196616 | tf_op jit(solution)/shard_map/ppermute | solution.py:64
  132.8 23.7 %copy-start.6 = (f32[1,256,128]{1,2,0:T(8,128)S(1)}, f32[1,256,128]{1,2,0:T(8,128)}, u32[]{:S(2)}) copy-start(f32[1,256,128]{1,2,0:T(8,128)} %maximum_bitcast_fusion.1) | copy-start | bytes 393220
  133.8 22.7 %copy-start.7 = (f32[1,256,128]{1,2,0:T(8,128)S(1)}, f32[1,256,128]{1,2,0:T(8,128)}, u32[]{:S(2)}) copy-start(f32[1,256,128]{1,2,0:T(8,128)} %maximum_bitcast_fusion.2) | copy-start | bytes 393220
  134.9 4.9 %collective-permute-start.54 = (f32[16,1280]{1,0:T(8,128)S(1)}, f32[16,1280]{1,0:T(8,128)S(1)}, u32[]{:S(2)}, u32[]{:S(2)}) collective-permute-start(f32[16,1280]{1,0:T(8,128)S(1)} %get-tuple-element.36), channel_id=1, source_target_pairs={{0,3},{1,0},{2,1},{3,2},{4,7},{5,4},{6,5},{7,6},{8,11},{9,8},{10,9... | collective-permute-start | bytes 245768 | tf_op jit(solution)/shard_map/ppermute | solution.py:21
  137.2 7.8 %collective-permute-start.53 = (f32[16,1280]{1,0:T(8,128)S(1)}, f32[16,1280]{1,0:T(8,128)S(1)}, u32[]{:S(2)}, u32[]{:S(2)}) collective-permute-start(f32[16,1280]{1,0:T(8,128)S(1)} %get-tuple-element.35), channel_id=1, source_target_pairs={{0,2},{1,3},{2,0},{3,1},{4,6},{5,7},{6,4},{7,5},{8,10},{9,11},{10,... | collective-permute-start | bytes 245768 | tf_op jit(solution)/shard_map/ppermute | solution.py:21
  137.4 7.6 %collective-permute-start.52 = (f32[16,1280]{1,0:T(8,128)S(1)}, f32[16,1280]{1,0:T(8,128)S(1)}, u32[]{:S(2)}, u32[]{:S(2)}) collective-permute-start(f32[16,1280]{1,0:T(8,128)S(1)} %get-tuple-element.34), channel_id=1, source_target_pairs={{0,1},{1,2},{2,3},{3,0},{4,5},{5,6},{6,7},{7,4},{8,9},{9,10},{10,1... | collective-permute-start | bytes 245768 | tf_op jit(solution)/shard_map/ppermute | solution.py:21
  146.8 6.8 %collective-permute-start.57 = (f32[16,256]{1,0:T(8,128)S(1)}, f32[16,256]{1,0:T(8,128)S(1)}, u32[]{:S(2)}, u32[]{:S(2)}) collective-permute-start(f32[16,256]{1,0:T(8,128)S(1)} %fusion.26), channel_id=1, source_target_pairs={{0,3},{1,0},{2,1},{3,2},{4,7},{5,4},{6,5},{7,6},{8,11},{9,8},{10,9... | collective-permute-start | bytes 49160 | tf_op jit(solution)/shard_map/ppermute | solution.py:21
  147.7 5.5 %collective-permute-start.55 = (f32[16,256]{1,0:T(8,128)S(1)}, f32[16,256]{1,0:T(8,128)S(1)}, u32[]{:S(2)}, u32[]{:S(2)}) collective-permute-start(f32[16,256]{1,0:T(8,128)S(1)} %fusion.26), channel_id=1, source_target_pairs={{0,1},{1,2},{2,3},{3,0},{4,5},{5,6},{6,7},{7,4},{8,9},{9,10},{10,1... | collective-permute-start | bytes 49160 | tf_op jit(solution)/shard_map/ppermute | solution.py:21
  148.8 4.9 %collective-permute-start.56 = (f32[16,256]{1,0:T(8,128)S(1)}, f32[16,256]{1,0:T(8,128)S(1)}, u32[]{:S(2)}, u32[]{:S(2)}) collective-permute-start(f32[16,256]{1,0:T(8,128)S(1)} %fusion.26), channel_id=1, source_target_pairs={{0,2},{1,3},{2,0},{3,1},{4,6},{5,7},{6,4},{7,5},{8,10},{9,11},{10,... | collective-permute-start | bytes 49160 | tf_op jit(solution)/shard_map/ppermute | solution.py:21
  154.0 6.0 %collective-permute-start.60 = (f32[16,256]{1,0:T(8,128)S(1)}, f32[16,256]{1,0:T(8,128)S(1)}, u32[]{:S(2)}, u32[]{:S(2)}) collective-permute-start(f32[16,256]{1,0:T(8,128)S(1)} %slice_subtract_fusion), channel_id=1, source_target_pairs={{0,3},{1,0},{2,1},{3,2},{4,7},{5,4},{6,5},{7,6},{8,11},{9,8},{10,9... | collective-permute-start | bytes 49160 | tf_op jit(solution)/shard_map/ppermute | solution.py:21
  159.4 4.6 %collective-permute-start.59 = (f32[16,256]{1,0:T(8,128)S(1)}, f32[16,256]{1,0:T(8,128)S(1)}, u32[]{:S(2)}, u32[]{:S(2)}) collective-permute-start(f32[16,256]{1,0:T(8,128)S(1)} %slice_subtract_fusion), channel_id=1, source_target_pairs={{0,2},{1,3},{2,0},{3,1},{4,6},{5,7},{6,4},{7,5},{8,10},{9,11},{10,... | collective-permute-start | bytes 49160 | tf_op jit(solution)/shard_map/ppermute | solution.py:21
  159.4 5.8 %collective-permute-start.58 = (f32[16,256]{1,0:T(8,128)S(1)}, f32[16,256]{1,0:T(8,128)S(1)}, u32[]{:S(2)}, u32[]{:S(2)}) collective-permute-start(f32[16,256]{1,0:T(8,128)S(1)} %slice_subtract_fusion), channel_id=1, source_target_pairs={{0,1},{1,2},{2,3},{3,0},{4,5},{5,6},{6,7},{7,4},{8,9},{9,10},{10,1... | collective-permute-start | bytes 49160 | tf_op jit(solution)/shard_map/ppermute | solution.py:21
  (10 other events, 112.6 us)

commit v6 on v5

--- a/solution.py
+++ b/solution.py
@@ -26,6 +26,15 @@
     me = lax.axis_index("grp")
     rows = value.shape[1]
     pieces = [(me * rows, value)]
+    if members == 4:
+        beside = lax.ppermute(value, "grp", [(0, 1), (1, 0), (2, 3), (3, 2)])
+        across = lax.ppermute(value, "grp", [(1, 2), (2, 1), (0, 3), (3, 0)])
+        inward = lax.ppermute(beside, "grp", [(1, 2), (2, 1)])
+        outward = lax.ppermute(across, "grp", [(1, 0), (2, 3)])
+        pieces.append(((me ^ 1) * rows, beside))
+        pieces.append(((me ^ 3) * rows, across))
+        pieces.append(((me ^ 2) * rows, inward + outward))
+        return pieces
     for shift in range(1, members):
         owner = lax.rem(me - shift + members, members)
         pieces.append((owner * rows, send(value, "grp", shift)))

time: 169 us -> 217 us (1.28); the launches traced: 168 us -> 213 us
  starting transfers between devices: 86.2 us -> 128 us
  waiting for transfers between devices: 23.6 us -> 29.1 us
  local copies, waits for them, and re-layouts: 12.1 us -> 9.74 us
    ppermute x0 -> x72, starting transfers between devices: none -> 118 us  [the longest x18 43.8 us: gather_rows(): beside = lax.ppermute(value, 'grp', [(0, 1), (1, 0), (2, 3), (3, 2)])]
    ppermute x57 -> x3, starting transfers between devices: 82.6 us -> 7.22 us  [send(): lax.ppermute(value, axis, [(i, (i + shift) % count) for i in range(count)])]
    ppermute x0 -> x72, waiting for transfers between devices: none -> 21.5 us  [the longest x18 11.5 us: gather_rows(): across = lax.ppermute(value, 'grp', [(1, 2), (2, 1), (0, 3), (3, 0)])]
    ppermute x57 -> x3, waiting for transfers between devices: 20.6 us -> 3.44 us  [send(): lax.ppermute(value, axis, [(i, (i + shift) % count) for i in range(count)])]
    unnamed x28 -> x20, local copies, waits for them, and re-layouts: 4.85 us -> 4.27 us
  transfers between devices with their start and end apart: 61 -> 79, of which waited for: 17 -> 16; matrix products, arithmetic and copies ran while one was open for 24% -> 19% of each run, Pallas kernels for 0% -> 0%
where the time goes in v6:
time: 217 us; the launch traced here: 213 us
  starting transfers between devices  128 us (59%)
  matrix products  36.9 us (17%)
  waiting for transfers between devices  29.1 us (13%)
  local copies, waits for them, and re-layouts  9.74 us (4%)
  other arithmetic  6.46 us (3%)
  between operations  2.8 us (1%)
    ppermute x18, starting transfers between devices, gather_rows(): beside = lax.ppermute(value, 'grp', [(0, 1), (1, 0), (2, 3), (3, 2)])  43.8 us
    ppermute x18, starting transfers between devices, gather_rows(): across = lax.ppermute(value, 'grp', [(1, 2), (2, 1), (0, 3), (3, 0)])  38.4 us
    dot_general x79, matrix products, contract_last(): lax.dot_general(left, right, (((left.ndim - 1,), (right.ndim - 1,)), ((),...  35.9 us
    ppermute x18, starting transfers between devices, gather_rows(): outward = lax.ppermute(across, 'grp', [(1, 0), (2, 3)])  23.2 us
    ppermute x18, starting transfers between devices, gather_rows(): inward = lax.ppermute(beside, 'grp', [(1, 2), (2, 1)])  12.2 us
    ppermute x18, waiting for transfers between devices, gather_rows(): across = lax.ppermute(value, 'grp', [(1, 2), (2, 1), (0, 3), (3, 0)])  11.5 us
    ppermute x18, waiting for transfers between devices, gather_rows(): outward = lax.ppermute(across, 'grp', [(1, 0), (2, 3)])  9.16 us
    ppermute x3, starting transfers between devices, send(): lax.ppermute(value, axis, [(i, (i + shift) % count) for i in range(count)])  7.22 us
  transfers between devices with their start and end apart: 79, of which 16 were waited for; matrix products, arithmetic and copies ran while one was open for 19% of the time, Pallas kernels for 0%

profile of v6, /device:TPU:0, one launch (start us, length us, event | category | flops | bytes accessed | tf_op | source)
XLA Modules:
  0.0 213.4 jit_solution(9060906445338953486)
XLA Ops:
  0.6 2.2 %copy.28 = f32[1,4,256,128]{2,3,1,0:T(8,128)} copy(f32[1,4,256,128]{3,2,1,0:T(8,128)} %param.12) | data formatting | bytes 1048576 | tf_op args[0]
  2.8 1.5 slice_bitcast_fusion.20
  4.4 3.0 %collective-permute-start = (f32[64,256]{1,0:T(8,128)}, f32[64,256]{1,0:T(8,128)S(1)}, u32[]{:S(2)}, u32[]{:S(2)}) collective-permute-start(f32[64,256]{1,0:T(8,128)} %get-tuple-element.20), channel_id=1, source_target_pairs={{0,1},{1,0},{2,3},{3,2},{4,5},{5,4},{6,7},{7,6},{8,9},{9,8},{10,11... | collective-permute-start | bytes 196616 | tf_op jit(solution)/shard_map/ppermute | solution.py:30
  7.4 2.5 %collective-permute-start.1 = (f32[64,256]{1,0:T(8,128)}, f32[64,256]{1,0:T(8,128)S(1)}, u32[]{:S(2)}, u32[]{:S(2)}) collective-permute-start(f32[64,256]{1,0:T(8,128)} %get-tuple-element.20), channel_id=1, source_target_pairs={{1,2},{2,1},{0,3},{3,0},{5,6},{6,5},{4,7},{7,4},{9,10},{10,9},{8,1... | collective-permute-start | bytes 196616 | tf_op jit(solution)/shard_map/ppermute | solution.py:31
  17.4 1.3 collective-permute-start.3
  20.7 1.3 convolution_add_fusion.44
  22.0 1.3 collective-permute-start.7
  24.5 1.4 fusion.6
  27.2 3.0 %collective-permute-start.9 = (f32[64,256]{1,0:T(8,128)S(1)}, f32[64,256]{1,0:T(8,128)S(1)}, u32[]{:S(2)}, u32[]{:S(2)}) collective-permute-start(f32[64,256]{1,0:T(8,128)S(1)} %get-tuple-element.44), channel_id=1, source_target_pairs={{1,2},{2,1},{0,3},{3,0},{5,6},{6,5},{4,7},{7,4},{9,10},{10,9},{8,1... | collective-permute-start | bytes 196616 | tf_op jit(solution)/shard_map/ppermute | solution.py:31
  30.2 4.1 %collective-permute-start.8 = (f32[64,256]{1,0:T(8,128)S(1)}, f32[64,256]{1,0:T(8,128)S(1)}, u32[]{:S(2)}, u32[]{:S(2)}) collective-permute-start(f32[64,256]{1,0:T(8,128)S(1)} %get-tuple-element.44), channel_id=1, source_target_pairs={{0,1},{1,0},{2,3},{3,2},{4,5},{5,4},{6,7},{7,6},{8,9},{9,8},{10,11... | collective-permute-start | bytes 196616 | tf_op jit(solution)/shard_map/ppermute | solution.py:30
  36.1 1.9 collective-permute-start.17
  38.0 1.3 collective-permute-start.11
  40.6 1.7 collective-permute-done.17
  42.3 1.3 collective-permute-start.19
  45.3 1.9 collective-permute-start.13
  47.2 4.7 %collective-permute-start.12 = (f32[64,256]{1,0:T(8,128)S(1)}, f32[64,256]{1,0:T(8,128)S(1)}, u32[]{:S(2)}, u32[]{:S(2)}) collective-permute-start(f32[64,256]{1,0:T(8,128)S(1)} %fusion.5), channel_id=1, source_target_pairs={{0,1},{1,0},{2,3},{3,2},{4,5},{5,4},{6,7},{7,6},{8,9},{9,8},{10,11... | collective-permute-start | bytes 196616 | tf_op jit(solution)/shard_map/ppermute | solution.py:30
  52.5 1.3 collective-permute-start.20
  54.2 2.0 collective-permute-start.21
  56.2 1.3 collective-permute-start.15
  58.7 1.6 collective-permute-done.21
  60.3 1.3 collective-permute-start.23
  63.5 2.0 collective-permute-start.25
  65.5 4.7 %collective-permute-start.24 = (f32[64,256]{1,0:T(8,128)S(1)}, f32[64,256]{1,0:T(8,128)S(1)}, u32[]{:S(2)}, u32[]{:S(2)}) collective-permute-start(f32[64,256]{1,0:T(8,128)S(1)} %get-tuple-element.46), channel_id=1, source_target_pairs={{0,1},{1,0},{2,3},{3,2},{4,5},{5,4},{6,7},{7,6},{8,9},{9,8},{10,11... | collective-permute-start | bytes 196616 | tf_op jit(solution)/shard_map/ppermute | solution.py:30
  70.8 2.0 collective-permute-start.33
  73.3 1.3 collective-permute-start.27
  77.0 1.3 collective-permute-start.35
  79.9 2.0 collective-permute-start.29
  81.9 5.1 %collective-permute-start.28 = (f32[64,256]{1,0:T(8,128)S(1)}, f32[64,256]{1,0:T(8,128)S(1)}, u32[]{:S(2)}, u32[]{:S(2)}) collective-permute-start(f32[64,256]{1,0:T(8,128)S(1)} %fusion.3), channel_id=1, source_target_pairs={{0,1},{1,0},{2,3},{3,2},{4,5},{5,4},{6,7},{7,6},{8,9},{9,8},{10,11... | collective-permute-start | bytes 196616 | tf_op jit(solution)/shard_map/ppermute | solution.py:30
  89.2 2.0 collective-permute-start.37
  91.2 1.3 collective-permute-start.31
  93.8 1.6 collective-permute-done.37
  95.4 1.3 collective-permute-start.39
  98.6 2.0 collective-permute-start.41
  100.7 4.5 %collective-permute-start.40 = (f32[64,256]{1,0:T(8,128)S(1)}, f32[64,256]{1,0:T(8,128)S(1)}, u32[]{:S(2)}, u32[]{:S(2)}) collective-permute-start(f32[64,256]{1,0:T(8,128)S(1)} %get-tuple-element.48), channel_id=1, source_target_pairs={{0,1},{1,0},{2,3},{3,2},{4,5},{5,4},{6,7},{7,6},{8,9},{9,8},{10,11... | collective-permute-start | bytes 196616 | tf_op jit(solution)/shard_map/ppermute | solution.py:30
  105.8 2.0 collective-permute-start.49
  108.4 1.3 collective-permute-start.43
  112.0 1.3 collective-permute-start.51
  115.4 2.0 collective-permute-start.45
  117.4 5.3 %collective-permute-start.44 = (f32[64,256]{1,0:T(8,128)S(1)}, f32[64,256]{1,0:T(8,128)S(1)}, u32[]{:S(2)}, u32[]{:S(2)}) collective-permute-start(f32[64,256]{1,0:T(8,128)S(1)} %fusion.1), channel_id=1, source_target_pairs={{0,1},{1,0},{2,3},{3,2},{4,5},{5,4},{6,7},{7,6},{8,9},{9,8},{10,11... | collective-permute-start | bytes 196616 | tf_op jit(solution)/shard_map/ppermute | solution.py:30
  126.2 2.1 collective-permute-start.53
  128.3 1.3 collective-permute-start.47
  130.9 1.6 collective-permute-done.53
  132.5 1.3 collective-permute-start.55
  136.0 2.0 collective-permute-start.57
  137.9 4.0 %collective-permute-start.56 = (f32[64,256]{1,0:T(8,128)S(1)}, f32[64,256]{1,0:T(8,128)S(1)}, u32[]{:S(2)}, u32[]{:S(2)}) collective-permute-start(f32[64,256]{1,0:T(8,128)S(1)} %convolution_add_fusion.12), channel_id=1, source_target_pairs={{0,1},{1,0},{2,3},{3,2},{4,5},{5,4},{6,7},{7,6},{8,9},{9,8},{10,11... | collective-permute-start | bytes 196616 | tf_op jit(solution)/shard_map/ppermute | solution.py:30
  142.2 2.1 collective-permute-start.61
  145.9 1.3 collective-permute-start.59
  148.5 1.3 collective-permute-start.63
  151.8 4.6 %collective-permute-done.63 = f32[64,256]{1,0:T(8,128)S(1)} collective-permute-done((f32[64,256]{1,0:T(8,128)S(1)}, f32[64,256]{1,0:T(8,128)S(1)}, u32[]{:S(2)}, u32[]{:S(2)}) %collective-permute-start.63) | collective-permute-done | bytes 65568 | tf_op jit(solution)/shard_map/ppermute | solution.py:33
  158.6 1.7 collective-permute-start.65
  160.3 1.5 collective-permute-start.66
  163.2 1.4 collective-permute-done.66
  164.6 2.4 %collective-permute-done.67 = f32[2,16,512]{2,1,0:T(8,128)S(1)} collective-permute-done((f32[2,16,512]{2,1,0:T(8,128)S(1)}, f32[2,16,512]{2,1,0:T(8,128)S(1)}, u32[]{:S(2)}, u32[]{:S(2)}) %collective-permute-start.67) | collective-permute-done | bytes 65568 | tf_op jit(solution)/shard_map/ppermute | solution.py:73
  172.0 4.0 %collective-permute-start.68 = (f32[16,1280]{1,0:T(8,128)S(1)}, f32[16,1280]{1,0:T(8,128)S(1)}, u32[]{:S(2)}, u32[]{:S(2)}) collective-permute-start(f32[16,1280]{1,0:T(8,128)S(1)} %get-tuple-element.34), channel_id=1, source_target_pairs={{0,1},{1,2},{2,3},{3,0},{4,5},{5,6},{6,7},{7,4},{8,9},{9,10},{10,1... | collective-permute-start | bytes 245768 | tf_op jit(solution)/shard_map/ppermute | solution.py:21
  176.3 2.8 %collective-permute-start.70 = (f32[16,1280]{1,0:T(8,128)S(1)}, f32[16,1280]{1,0:T(8,128)S(1)}, u32[]{:S(2)}, u32[]{:S(2)}) collective-permute-start(f32[16,1280]{1,0:T(8,128)S(1)} %get-tuple-element.36), channel_id=1, source_target_pairs={{0,3},{1,0},{2,1},{3,2},{4,7},{5,4},{6,5},{7,6},{8,11},{9,8},{10,9... | collective-permute-start | bytes 245768 | tf_op jit(solution)/shard_map/ppermute | solution.py:21
  179.2 3.4 %collective-permute-done.69 = f32[16,1280]{1,0:T(8,128)S(1)} collective-permute-done((f32[16,1280]{1,0:T(8,128)S(1)}, f32[16,1280]{1,0:T(8,128)S(1)}, u32[]{:S(2)}, u32[]{:S(2)}) %collective-permute-start.69) | collective-permute-done | bytes 81952 | tf_op jit(solution)/shard_map/ppermute | solution.py:21
  182.7 1.7 fusion.11
  184.4 3.0 %collective-permute-start.72 = (f32[16,256]{1,0:T(8,128)S(1)}, f32[16,256]{1,0:T(8,128)S(1)}, u32[]{:S(2)}, u32[]{:S(2)}) collective-permute-start(f32[16,256]{1,0:T(8,128)S(1)} %fusion.11), channel_id=1, source_target_pairs={{1,2},{2,1},{0,3},{3,0},{5,6},{6,5},{4,7},{7,4},{9,10},{10,9},{8,1... | collective-permute-start | bytes 49160 | tf_op jit(solution)/shard_map/ppermute | solution.py:31
  187.6 2.4 %collective-permute-done.72 = f32[16,256]{1,0:T(8,128)S(1)} collective-permute-done((f32[16,256]{1,0:T(8,128)S(1)}, f32[16,256]{1,0:T(8,128)S(1)}, u32[]{:S(2)}, u32[]{:S(2)}) %collective-permute-start.72) | collective-permute-done | bytes 16416 | tf_op jit(solution)/shard_map/ppermute | solution.py:31
  192.4 3.2 %collective-permute-done.74 = f32[16,256]{1,0:T(8,128)S(1)} collective-permute-done((f32[16,256]{1,0:T(8,128)S(1)}, f32[16,256]{1,0:T(8,128)S(1)}, u32[]{:S(2)}, u32[]{:S(2)}) %collective-permute-start.74) | collective-permute-done | bytes 16416 | tf_op jit(solution)/shard_map/ppermute | solution.py:33
  195.8 3.0 %collective-permute-start.76 = (f32[16,256]{1,0:T(8,128)S(1)}, f32[16,256]{1,0:T(8,128)S(1)}, u32[]{:S(2)}, u32[]{:S(2)}) collective-permute-start(f32[16,256]{1,0:T(8,128)S(1)} %fusion.10), channel_id=1, source_target_pairs={{1,2},{2,1},{0,3},{3,0},{5,6},{6,5},{4,7},{7,4},{9,10},{10,9},{8,1... | collective-permute-start | bytes 49160 | tf_op jit(solution)/shard_map/ppermute | solution.py:31
  199.6 2.0 copy.32
  201.7 3.0 %collective-permute-start.75 = (f32[16,256]{1,0:T(8,128)S(1)}, f32[16,256]{1,0:T(8,128)S(1)}, u32[]{:S(2)}, u32[]{:S(2)}) collective-permute-start(f32[16,256]{1,0:T(8,128)S(1)} %fusion.10), channel_id=1, source_target_pairs={{0,1},{1,0},{2,3},{3,2},{4,5},{5,4},{6,7},{7,6},{8,9},{9,8},{10,11... | collective-permute-start | bytes 49160 | tf_op jit(solution)/shard_map/ppermute | solution.py:30
  205.8 1.4 collective-permute-start.78
  (249 shorter events, 67.2 us)
Async XLA Ops:
  4.4 12.4 %collective-permute-start = (f32[64,256]{1,0:T(8,128)}, f32[64,256]{1,0:T(8,128)S(1)}, u32[]{:S(2)}, u32[]{:S(2)}) collective-permute-start(f32[64,256]{1,0:T(8,128)} %get-tuple-element.20), channel_id=1, source_target_pairs={{0,1},{1,0},{2,3},{3,2},{4,5},{5,4},{6,7},{7,6},{8,9},{9,8},{10,11... | collective-permute-start | bytes 196616 | tf_op jit(solution)/shard_map/ppermute | solution.py:30
  7.4 10.1 %collective-permute-start.1 = (f32[64,256]{1,0:T(8,128)}, f32[64,256]{1,0:T(8,128)S(1)}, u32[]{:S(2)}, u32[]{:S(2)}) collective-permute-start(f32[64,256]{1,0:T(8,128)} %get-tuple-element.20), channel_id=1, source_target_pairs={{1,2},{2,1},{0,3},{3,0},{5,6},{6,5},{4,7},{7,4},{9,10},{10,9},{8,1... | collective-permute-start | bytes 196616 | tf_op jit(solution)/shard_map/ppermute | solution.py:31
  9.9 8.9 %collective-permute-start.4 = (f32[64,256]{1,0:T(8,128)}, f32[64,256]{1,0:T(8,128)S(1)}, u32[]{:S(2)}, u32[]{:S(2)}) collective-permute-start(f32[64,256]{1,0:T(8,128)} %get-tuple-element.21), channel_id=1, source_target_pairs={{0,1},{1,0},{2,3},{3,2},{4,5},{5,4},{6,7},{7,6},{8,9},{9,8},{10,11... | collective-permute-start | bytes 196616 | tf_op jit(solution)/shard_map/ppermute | solution.py:30
  10.5 11.4 %collective-permute-start.5 = (f32[64,256]{1,0:T(8,128)}, f32[64,256]{1,0:T(8,128)S(1)}, u32[]{:S(2)}, u32[]{:S(2)}) collective-permute-start(f32[64,256]{1,0:T(8,128)} %get-tuple-element.21), channel_id=1, source_target_pairs={{1,2},{2,1},{0,3},{3,0},{5,6},{6,5},{4,7},{7,4},{9,10},{10,9},{8,1... | collective-permute-start | bytes 196616 | tf_op jit(solution)/shard_map/ppermute | solution.py:31
  16.8 9.2 %collective-permute-start.2 = (f32[64,256]{1,0:T(8,128)S(1)}, f32[64,256]{1,0:T(8,128)S(1)}, u32[]{:S(2)}, u32[]{:S(2)}) collective-permute-start(f32[64,256]{1,0:T(8,128)S(1)} %collective-permute-done), channel_id=1, source_target_pairs={{1,2},{2,1},{5,6},{6,5},{9,10},{10,9},{13,14},{14,13},{17,18},{18,... | collective-permute-start | bytes 196616 | tf_op jit(solution)/shard_map/ppermute | solution.py:32
  17.4 8.5 %collective-permute-start.3 = (f32[64,256]{1,0:T(8,128)S(1)}, f32[64,256]{1,0:T(8,128)S(1)}, u32[]{:S(2)}, u32[]{:S(2)}) collective-permute-start(f32[64,256]{1,0:T(8,128)S(1)} %collective-permute-done.1), channel_id=1, source_target_pairs={{1,0},{2,3},{5,4},{6,7},{9,8},{10,11},{13,12},{14,15},{17,16},{18,... | collective-permute-start | bytes 196616 | tf_op jit(solution)/shard_map/ppermute | solution.py:33
  18.8 15.8 %collective-permute-start.6 = (f32[64,256]{1,0:T(8,128)S(1)}, f32[64,256]{1,0:T(8,128)S(1)}, u32[]{:S(2)}, u32[]{:S(2)}) collective-permute-start(f32[64,256]{1,0:T(8,128)S(1)} %collective-permute-done.4), channel_id=1, source_target_pairs={{1,2},{2,1},{5,6},{6,5},{9,10},{10,9},{13,14},{14,13},{17,18},{18,... | collective-permute-start | bytes 196616 | tf_op jit(solution)/shard_map/ppermute | solution.py:32
  22.0 12.6 %collective-permute-start.7 = (f32[64,256]{1,0:T(8,128)S(1)}, f32[64,256]{1,0:T(8,128)S(1)}, u32[]{:S(2)}, u32[]{:S(2)}) collective-permute-start(f32[64,256]{1,0:T(8,128)S(1)} %collective-permute-done.5), channel_id=1, source_target_pairs={{1,0},{2,3},{5,4},{6,7},{9,8},{10,11},{13,12},{14,15},{17,16},{18,... | collective-permute-start | bytes 196616 | tf_op jit(solution)/shard_map/ppermute | solution.py:33
  27.2 10.8 %collective-permute-start.9 = (f32[64,256]{1,0:T(8,128)S(1)}, f32[64,256]{1,0:T(8,128)S(1)}, u32[]{:S(2)}, u32[]{:S(2)}) collective-permute-start(f32[64,256]{1,0:T(8,128)S(1)} %get-tuple-element.44), channel_id=1, source_target_pairs={{1,2},{2,1},{0,3},{3,0},{5,6},{6,5},{4,7},{7,4},{9,10},{10,9},{8,1... | collective-permute-start | bytes 196616 | tf_op jit(solution)/shard_map/ppermute | solution.py:31
  30.2 9.1 %collective-permute-start.8 = (f32[64,256]{1,0:T(8,128)S(1)}, f32[64,256]{1,0:T(8,128)S(1)}, u32[]{:S(2)}, u32[]{:S(2)}) collective-permute-start(f32[64,256]{1,0:T(8,128)S(1)} %get-tuple-element.44), channel_id=1, source_target_pairs={{0,1},{1,0},{2,3},{3,2},{4,5},{5,4},{6,7},{7,6},{8,9},{9,8},{10,11... | collective-permute-start | bytes 196616 | tf_op jit(solution)/shard_map/ppermute | solution.py:30
  36.1 6.2 %collective-permute-start.17 = (f32[64,256]{1,0:T(8,128)S(1)}, f32[64,256]{1,0:T(8,128)S(1)}, u32[]{:S(2)}, u32[]{:S(2)}) collective-permute-start(f32[64,256]{1,0:T(8,128)S(1)} %get-tuple-element.50), channel_id=1, source_target_pairs={{1,2},{2,1},{0,3},{3,0},{5,6},{6,5},{4,7},{7,4},{9,10},{10,9},{8,1... | collective-permute-start | bytes 196616 | tf_op jit(solution)/shard_map/ppermute | solution.py:31
  38.0 5.6 %collective-permute-start.16 = (f32[64,256]{1,0:T(8,128)S(1)}, f32[64,256]{1,0:T(8,128)S(1)}, u32[]{:S(2)}, u32[]{:S(2)}) collective-permute-start(f32[64,256]{1,0:T(8,128)S(1)} %get-tuple-element.50), channel_id=1, source_target_pairs={{0,1},{1,0},{2,3},{3,2},{4,5},{5,4},{6,7},{7,6},{8,9},{9,8},{10,11... | collective-permute-start | bytes 196616 | tf_op jit(solution)/shard_map/ppermute | solution.py:30
  38.0 6.9 %collective-permute-start.11 = (f32[64,256]{1,0:T(8,128)S(1)}, f32[64,256]{1,0:T(8,128)S(1)}, u32[]{:S(2)}, u32[]{:S(2)}) collective-permute-start(f32[64,256]{1,0:T(8,128)S(1)} %collective-permute-done.9), channel_id=1, source_target_pairs={{1,0},{2,3},{5,4},{6,7},{9,8},{10,11},{13,12},{14,15},{17,16},{18,... | collective-permute-start | bytes 196616 | tf_op jit(solution)/shard_map/ppermute | solution.py:33
  39.3 5.6 %collective-permute-start.10 = (f32[64,256]{1,0:T(8,128)S(1)}, f32[64,256]{1,0:T(8,128)S(1)}, u32[]{:S(2)}, u32[]{:S(2)}) collective-permute-start(f32[64,256]{1,0:T(8,128)S(1)} %collective-permute-done.8), channel_id=1, source_target_pairs={{1,2},{2,1},{5,6},{6,5},{9,10},{10,9},{13,14},{14,13},{17,18},{18,... | collective-permute-start | bytes 196616 | tf_op jit(solution)/shard_map/ppermute | solution.py:32
  42.3 9.6 %collective-permute-start.19 = (f32[64,256]{1,0:T(8,128)S(1)}, f32[64,256]{1,0:T(8,128)S(1)}, u32[]{:S(2)}, u32[]{:S(2)}) collective-permute-start(f32[64,256]{1,0:T(8,128)S(1)} %collective-permute-done.17), channel_id=1, source_target_pairs={{1,0},{2,3},{5,4},{6,7},{9,8},{10,11},{13,12},{14,15},{17,16},{18,... | collective-permute-start | bytes 196616 | tf_op jit(solution)/shard_map/ppermute | solution.py:33
  43.6 8.3 %collective-permute-start.18 = (f32[64,256]{1,0:T(8,128)S(1)}, f32[64,256]{1,0:T(8,128)S(1)}, u32[]{:S(2)}, u32[]{:S(2)}) collective-permute-start(f32[64,256]{1,0:T(8,128)S(1)} %collective-permute-done.16), channel_id=1, source_target_pairs={{1,2},{2,1},{5,6},{6,5},{9,10},{10,9},{13,14},{14,13},{17,18},{18,... | collective-permute-start | bytes 196616 | tf_op jit(solution)/shard_map/ppermute | solution.py:32
  45.3 10.9 %collective-permute-start.13 = (f32[64,256]{1,0:T(8,128)S(1)}, f32[64,256]{1,0:T(8,128)S(1)}, u32[]{:S(2)}, u32[]{:S(2)}) collective-permute-start(f32[64,256]{1,0:T(8,128)S(1)} %fusion.5), channel_id=1, source_target_pairs={{1,2},{2,1},{0,3},{3,0},{5,6},{6,5},{4,7},{7,4},{9,10},{10,9},{8,1... | collective-permute-start | bytes 196616 | tf_op jit(solution)/shard_map/ppermute | solution.py:31
  47.2 10.3 %collective-permute-start.12 = (f32[64,256]{1,0:T(8,128)S(1)}, f32[64,256]{1,0:T(8,128)S(1)}, u32[]{:S(2)}, u32[]{:S(2)}) collective-permute-start(f32[64,256]{1,0:T(8,128)S(1)} %fusion.5), channel_id=1, source_target_pairs={{0,1},{1,0},{2,3},{3,2},{4,5},{5,4},{6,7},{7,6},{8,9},{9,8},{10,11... | collective-permute-start | bytes 196616 | tf_op jit(solution)/shard_map/ppermute | solution.py:30
  52.5 9.1 %collective-permute-start.20 = (f32[64,256]{1,0:T(8,128)S(1)}, f32[64,256]{1,0:T(8,128)S(1)}, u32[]{:S(2)}, u32[]{:S(2)}) collective-permute-start(f32[64,256]{1,0:T(8,128)S(1)} %fusion.4), channel_id=1, source_target_pairs={{0,1},{1,0},{2,3},{3,2},{4,5},{5,4},{6,7},{7,6},{8,9},{9,8},{10,11... | collective-permute-start | bytes 196616 | tf_op jit(solution)/shard_map/ppermute | solution.py:30
  54.2 6.1 %collective-permute-start.21 = (f32[64,256]{1,0:T(8,128)S(1)}, f32[64,256]{1,0:T(8,128)S(1)}, u32[]{:S(2)}, u32[]{:S(2)}) collective-permute-start(f32[64,256]{1,0:T(8,128)S(1)} %fusion.4), channel_id=1, source_target_pairs={{1,2},{2,1},{0,3},{3,0},{5,6},{6,5},{4,7},{7,4},{9,10},{10,9},{8,1... | collective-permute-start | bytes 196616 | tf_op jit(solution)/shard_map/ppermute | solution.py:31
  56.2 6.7 %collective-permute-start.15 = (f32[64,256]{1,0:T(8,128)S(1)}, f32[64,256]{1,0:T(8,128)S(1)}, u32[]{:S(2)}, u32[]{:S(2)}) collective-permute-start(f32[64,256]{1,0:T(8,128)S(1)} %collective-permute-done.13), channel_id=1, source_target_pairs={{1,0},{2,3},{5,4},{6,7},{9,8},{10,11},{13,12},{14,15},{17,16},{18,... | collective-permute-start | bytes 196616 | tf_op jit(solution)/shard_map/ppermute | solution.py:33
  60.3 9.9 %collective-permute-start.23 = (f32[64,256]{1,0:T(8,128)S(1)}, f32[64,256]{1,0:T(8,128)S(1)}, u32[]{:S(2)}, u32[]{:S(2)}) collective-permute-start(f32[64,256]{1,0:T(8,128)S(1)} %collective-permute-done.21), channel_id=1, source_target_pairs={{1,0},{2,3},{5,4},{6,7},{9,8},{10,11},{13,12},{14,15},{17,16},{18,... | collective-permute-start | bytes 196616 | tf_op jit(solution)/shard_map/ppermute | solution.py:33
  61.6 8.6 %collective-permute-start.22 = (f32[64,256]{1,0:T(8,128)S(1)}, f32[64,256]{1,0:T(8,128)S(1)}, u32[]{:S(2)}, u32[]{:S(2)}) collective-permute-start(f32[64,256]{1,0:T(8,128)S(1)} %collective-permute-done.20), channel_id=1, source_target_pairs={{1,2},{2,1},{5,6},{6,5},{9,10},{10,9},{13,14},{14,13},{17,18},{18,... | collective-permute-start | bytes 196616 | tf_op jit(solution)/shard_map/ppermute | solution.py:32
  63.5 9.8 %collective-permute-start.25 = (f32[64,256]{1,0:T(8,128)S(1)}, f32[64,256]{1,0:T(8,128)S(1)}, u32[]{:S(2)}, u32[]{:S(2)}) collective-permute-start(f32[64,256]{1,0:T(8,128)S(1)} %get-tuple-element.46), channel_id=1, source_target_pairs={{1,2},{2,1},{0,3},{3,0},{5,6},{6,5},{4,7},{7,4},{9,10},{10,9},{8,1... | collective-permute-start | bytes 196616 | tf_op jit(solution)/shard_map/ppermute | solution.py:31
  65.5 9.1 %collective-permute-start.24 = (f32[64,256]{1,0:T(8,128)S(1)}, f32[64,256]{1,0:T(8,128)S(1)}, u32[]{:S(2)}, u32[]{:S(2)}) collective-permute-start(f32[64,256]{1,0:T(8,128)S(1)} %get-tuple-element.46), channel_id=1, source_target_pairs={{0,1},{1,0},{2,3},{3,2},{4,5},{5,4},{6,7},{7,6},{8,9},{9,8},{10,11... | collective-permute-start | bytes 196616 | tf_op jit(solution)/shard_map/ppermute | solution.py:30
  70.8 6.2 %collective-permute-start.33 = (f32[64,256]{1,0:T(8,128)S(1)}, f32[64,256]{1,0:T(8,128)S(1)}, u32[]{:S(2)}, u32[]{:S(2)}) collective-permute-start(f32[64,256]{1,0:T(8,128)S(1)} %get-tuple-element.52), channel_id=1, source_target_pairs={{1,2},{2,1},{0,3},{3,0},{5,6},{6,5},{4,7},{7,4},{9,10},{10,9},{8,1... | collective-permute-start | bytes 196616 | tf_op jit(solution)/shard_map/ppermute | solution.py:31
  73.3 6.3 %collective-permute-start.27 = (f32[64,256]{1,0:T(8,128)S(1)}, f32[64,256]{1,0:T(8,128)S(1)}, u32[]{:S(2)}, u32[]{:S(2)}) collective-permute-start(f32[64,256]{1,0:T(8,128)S(1)} %collective-permute-done.25), channel_id=1, source_target_pairs={{1,0},{2,3},{5,4},{6,7},{9,8},{10,11},{13,12},{14,15},{17,16},{18,... | collective-permute-start | bytes 196616 | tf_op jit(solution)/shard_map/ppermute | solution.py:33
  77.0 10.1 %collective-permute-start.35 = (f32[64,256]{1,0:T(8,128)S(1)}, f32[64,256]{1,0:T(8,128)S(1)}, u32[]{:S(2)}, u32[]{:S(2)}) collective-permute-start(f32[64,256]{1,0:T(8,128)S(1)} %collective-permute-done.33), channel_id=1, source_target_pairs={{1,0},{2,3},{5,4},{6,7},{9,8},{10,11},{13,12},{14,15},{17,16},{18,... | collective-permute-start | bytes 196616 | tf_op jit(solution)/shard_map/ppermute | solution.py:33
  78.3 8.8 %collective-permute-start.34 = (f32[64,256]{1,0:T(8,128)S(1)}, f32[64,256]{1,0:T(8,128)S(1)}, u32[]{:S(2)}, u32[]{:S(2)}) collective-permute-start(f32[64,256]{1,0:T(8,128)S(1)} %collective-permute-done.32), channel_id=1, source_target_pairs={{1,2},{2,1},{5,6},{6,5},{9,10},{10,9},{13,14},{14,13},{17,18},{18,... | collective-permute-start | bytes 196616 | tf_op jit(solution)/shard_map/ppermute | solution.py:32
  79.9 11.3 %collective-permute-start.29 = (f32[64,256]{1,0:T(8,128)S(1)}, f32[64,256]{1,0:T(8,128)S(1)}, u32[]{:S(2)}, u32[]{:S(2)}) collective-permute-start(f32[64,256]{1,0:T(8,128)S(1)} %fusion.3), channel_id=1, source_target_pairs={{1,2},{2,1},{0,3},{3,0},{5,6},{6,5},{4,7},{7,4},{9,10},{10,9},{8,1... | collective-permute-start | bytes 196616 | tf_op jit(solution)/shard_map/ppermute | solution.py:31
  81.9 10.6 %collective-permute-start.28 = (f32[64,256]{1,0:T(8,128)S(1)}, f32[64,256]{1,0:T(8,128)S(1)}, u32[]{:S(2)}, u32[]{:S(2)}) collective-permute-start(f32[64,256]{1,0:T(8,128)S(1)} %fusion.3), channel_id=1, source_target_pairs={{0,1},{1,0},{2,3},{3,2},{4,5},{5,4},{6,7},{7,6},{8,9},{9,8},{10,11... | collective-permute-start | bytes 196616 | tf_op jit(solution)/shard_map/ppermute | solution.py:30
  87.6 9.1 %collective-permute-start.36 = (f32[64,256]{1,0:T(8,128)S(1)}, f32[64,256]{1,0:T(8,128)S(1)}, u32[]{:S(2)}, u32[]{:S(2)}) collective-permute-start(f32[64,256]{1,0:T(8,128)S(1)} %fusion.2), channel_id=1, source_target_pairs={{0,1},{1,0},{2,3},{3,2},{4,5},{5,4},{6,7},{7,6},{8,9},{9,8},{10,11... | collective-permute-start | bytes 196616 | tf_op jit(solution)/shard_map/ppermute | solution.py:30
  89.2 6.2 %collective-permute-start.37 = (f32[64,256]{1,0:T(8,128)S(1)}, f32[64,256]{1,0:T(8,128)S(1)}, u32[]{:S(2)}, u32[]{:S(2)}) collective-permute-start(f32[64,256]{1,0:T(8,128)S(1)} %fusion.2), channel_id=1, source_target_pairs={{1,2},{2,1},{0,3},{3,0},{5,6},{6,5},{4,7},{7,4},{9,10},{10,9},{8,1... | collective-permute-start | bytes 196616 | tf_op jit(solution)/shard_map/ppermute | solution.py:31
  91.2 6.8 %collective-permute-start.31 = (f32[64,256]{1,0:T(8,128)S(1)}, f32[64,256]{1,0:T(8,128)S(1)}, u32[]{:S(2)}, u32[]{:S(2)}) collective-permute-start(f32[64,256]{1,0:T(8,128)S(1)} %collective-permute-done.29), channel_id=1, source_target_pairs={{1,0},{2,3},{5,4},{6,7},{9,8},{10,11},{13,12},{14,15},{17,16},{18,... | collective-permute-start | bytes 196616 | tf_op jit(solution)/shard_map/ppermute | solution.py:33
  95.4 9.8 %collective-permute-start.39 = (f32[64,256]{1,0:T(8,128)S(1)}, f32[64,256]{1,0:T(8,128)S(1)}, u32[]{:S(2)}, u32[]{:S(2)}) collective-permute-start(f32[64,256]{1,0:T(8,128)S(1)} %collective-permute-done.37), channel_id=1, source_target_pairs={{1,0},{2,3},{5,4},{6,7},{9,8},{10,11},{13,12},{14,15},{17,16},{18,... | collective-permute-start | bytes 196616 | tf_op jit(solution)/shard_map/ppermute | solution.py:33
  96.7 8.5 %collective-permute-start.38 = (f32[64,256]{1,0:T(8,128)S(1)}, f32[64,256]{1,0:T(8,128)S(1)}, u32[]{:S(2)}, u32[]{:S(2)}) collective-permute-start(f32[64,256]{1,0:T(8,128)S(1)} %collective-permute-done.36), channel_id=1, source_target_pairs={{1,2},{2,1},{5,6},{6,5},{9,10},{10,9},{13,14},{14,13},{17,18},{18,... | collective-permute-start | bytes 196616 | tf_op jit(solution)/shard_map/ppermute | solution.py:32
  98.6 9.8 %collective-permute-start.41 = (f32[64,256]{1,0:T(8,128)S(1)}, f32[64,256]{1,0:T(8,128)S(1)}, u32[]{:S(2)}, u32[]{:S(2)}) collective-permute-start(f32[64,256]{1,0:T(8,128)S(1)} %get-tuple-element.48), channel_id=1, source_target_pairs={{1,2},{2,1},{0,3},{3,0},{5,6},{6,5},{4,7},{7,4},{9,10},{10,9},{8,1... | collective-permute-start | bytes 196616 | tf_op jit(solution)/shard_map/ppermute | solution.py:31
  100.7 9.1 %collective-permute-start.40 = (f32[64,256]{1,0:T(8,128)S(1)}, f32[64,256]{1,0:T(8,128)S(1)}, u32[]{:S(2)}, u32[]{:S(2)}) collective-permute-start(f32[64,256]{1,0:T(8,128)S(1)} %get-tuple-element.48), channel_id=1, source_target_pairs={{0,1},{1,0},{2,3},{3,2},{4,5},{5,4},{6,7},{7,6},{8,9},{9,8},{10,11... | collective-permute-start | bytes 196616 | tf_op jit(solution)/shard_map/ppermute | solution.py:30
  105.8 6.2 %collective-permute-start.49 = (f32[64,256]{1,0:T(8,128)S(1)}, f32[64,256]{1,0:T(8,128)S(1)}, u32[]{:S(2)}, u32[]{:S(2)}) collective-permute-start(f32[64,256]{1,0:T(8,128)S(1)} %get-tuple-element.54), channel_id=1, source_target_pairs={{1,2},{2,1},{0,3},{3,0},{5,6},{6,5},{4,7},{7,4},{9,10},{10,9},{8,1... | collective-permute-start | bytes 196616 | tf_op jit(solution)/shard_map/ppermute | solution.py:31
  108.4 6.4 %collective-permute-start.43 = (f32[64,256]{1,0:T(8,128)S(1)}, f32[64,256]{1,0:T(8,128)S(1)}, u32[]{:S(2)}, u32[]{:S(2)}) collective-permute-start(f32[64,256]{1,0:T(8,128)S(1)} %collective-permute-done.41), channel_id=1, source_target_pairs={{1,0},{2,3},{5,4},{6,7},{9,8},{10,11},{13,12},{14,15},{17,16},{18,... | collective-permute-start | bytes 196616 | tf_op jit(solution)/shard_map/ppermute | solution.py:33
  112.0 10.7 %collective-permute-start.51 = (f32[64,256]{1,0:T(8,128)S(1)}, f32[64,256]{1,0:T(8,128)S(1)}, u32[]{:S(2)}, u32[]{:S(2)}) collective-permute-start(f32[64,256]{1,0:T(8,128)S(1)} %collective-permute-done.49), channel_id=1, source_target_pairs={{1,0},{2,3},{5,4},{6,7},{9,8},{10,11},{13,12},{14,15},{17,16},{18,... | collective-permute-start | bytes 196616 | tf_op jit(solution)/shard_map/ppermute | solution.py:33
  113.3 9.4 %collective-permute-start.50 = (f32[64,256]{1,0:T(8,128)S(1)}, f32[64,256]{1,0:T(8,128)S(1)}, u32[]{:S(2)}, u32[]{:S(2)}) collective-permute-start(f32[64,256]{1,0:T(8,128)S(1)} %collective-permute-done.48), channel_id=1, source_target_pairs={{1,2},{2,1},{5,6},{6,5},{9,10},{10,9},{13,14},{14,13},{17,18},{18,... | collective-permute-start | bytes 196616 | tf_op jit(solution)/shard_map/ppermute | solution.py:32
  115.4 12.9 %collective-permute-start.45 = (f32[64,256]{1,0:T(8,128)S(1)}, f32[64,256]{1,0:T(8,128)S(1)}, u32[]{:S(2)}, u32[]{:S(2)}) collective-permute-start(f32[64,256]{1,0:T(8,128)S(1)} %fusion.1), channel_id=1, source_target_pairs={{1,2},{2,1},{0,3},{3,0},{5,6},{6,5},{4,7},{7,4},{9,10},{10,9},{8,1... | collective-permute-start | bytes 196616 | tf_op jit(solution)/shard_map/ppermute | solution.py:31
  117.4 12.2 %collective-permute-start.44 = (f32[64,256]{1,0:T(8,128)S(1)}, f32[64,256]{1,0:T(8,128)S(1)}, u32[]{:S(2)}, u32[]{:S(2)}) collective-permute-start(f32[64,256]{1,0:T(8,128)S(1)} %fusion.1), channel_id=1, source_target_pairs={{0,1},{1,0},{2,3},{3,2},{4,5},{5,4},{6,7},{7,6},{8,9},{9,8},{10,11... | collective-permute-start | bytes 196616 | tf_op jit(solution)/shard_map/ppermute | solution.py:30
  126.2 6.3 %collective-permute-start.53 = (f32[64,256]{1,0:T(8,128)S(1)}, f32[64,256]{1,0:T(8,128)S(1)}, u32[]{:S(2)}, u32[]{:S(2)}) collective-permute-start(f32[64,256]{1,0:T(8,128)S(1)} %fusion), channel_id=1, source_target_pairs={{1,2},{2,1},{0,3},{3,0},{5,6},{6,5},{4,7},{7,4},{9,10},{10,9},{8,1... | collective-permute-start | bytes 196616 | tf_op jit(solution)/shard_map/ppermute | solution.py:31
  128.3 6.1 %collective-permute-start.52 = (f32[64,256]{1,0:T(8,128)S(1)}, f32[64,256]{1,0:T(8,128)S(1)}, u32[]{:S(2)}, u32[]{:S(2)}) collective-permute-start(f32[64,256]{1,0:T(8,128)S(1)} %fusion), channel_id=1, source_target_pairs={{0,1},{1,0},{2,3},{3,2},{4,5},{5,4},{6,7},{7,6},{8,9},{9,8},{10,11... | collective-permute-start | bytes 196616 | tf_op jit(solution)/shard_map/ppermute | solution.py:30
  128.3 7.3 %collective-permute-start.47 = (f32[64,256]{1,0:T(8,128)S(1)}, f32[64,256]{1,0:T(8,128)S(1)}, u32[]{:S(2)}, u32[]{:S(2)}) collective-permute-start(f32[64,256]{1,0:T(8,128)S(1)} %collective-permute-done.45), channel_id=1, source_target_pairs={{1,0},{2,3},{5,4},{6,7},{9,8},{10,11},{13,12},{14,15},{17,16},{18,... | collective-permute-start | bytes 196616 | tf_op jit(solution)/shard_map/ppermute | solution.py:33
  129.6 6.0 %collective-permute-start.46 = (f32[64,256]{1,0:T(8,128)S(1)}, f32[64,256]{1,0:T(8,128)S(1)}, u32[]{:S(2)}, u32[]{:S(2)}) collective-permute-start(f32[64,256]{1,0:T(8,128)S(1)} %collective-permute-done.44), channel_id=1, source_target_pairs={{1,2},{2,1},{5,6},{6,5},{9,10},{10,9},{13,14},{14,13},{17,18},{18,... | collective-permute-start | bytes 196616 | tf_op jit(solution)/shard_map/ppermute | solution.py:32
  132.5 9.4 %collective-permute-start.55 = (f32[64,256]{1,0:T(8,128)S(1)}, f32[64,256]{1,0:T(8,128)S(1)}, u32[]{:S(2)}, u32[]{:S(2)}) collective-permute-start(f32[64,256]{1,0:T(8,128)S(1)} %collective-permute-done.53), channel_id=1, source_target_pairs={{1,0},{2,3},{5,4},{6,7},{9,8},{10,11},{13,12},{14,15},{17,16},{18,... | collective-permute-start | bytes 196616 | tf_op jit(solution)/shard_map/ppermute | solution.py:33
  134.4 7.5 %collective-permute-start.54 = (f32[64,256]{1,0:T(8,128)S(1)}, f32[64,256]{1,0:T(8,128)S(1)}, u32[]{:S(2)}, u32[]{:S(2)}) collective-permute-start(f32[64,256]{1,0:T(8,128)S(1)} %collective-permute-done.52), channel_id=1, source_target_pairs={{1,2},{2,1},{5,6},{6,5},{9,10},{10,9},{13,14},{14,13},{17,18},{18,... | collective-permute-start | bytes 196616 | tf_op jit(solution)/shard_map/ppermute | solution.py:32
  136.0 10.0 %collective-permute-start.57 = (f32[64,256]{1,0:T(8,128)S(1)}, f32[64,256]{1,0:T(8,128)S(1)}, u32[]{:S(2)}, u32[]{:S(2)}) collective-permute-start(f32[64,256]{1,0:T(8,128)S(1)} %convolution_add_fusion.12), channel_id=1, source_target_pairs={{1,2},{2,1},{0,3},{3,0},{5,6},{6,5},{4,7},{7,4},{9,10},{10,9},{8,1... | collective-permute-start | bytes 196616 | tf_op jit(solution)/shard_map/ppermute | solution.py:31
  137.9 9.3 %collective-permute-start.56 = (f32[64,256]{1,0:T(8,128)S(1)}, f32[64,256]{1,0:T(8,128)S(1)}, u32[]{:S(2)}, u32[]{:S(2)}) collective-permute-start(f32[64,256]{1,0:T(8,128)S(1)} %convolution_add_fusion.12), channel_id=1, source_target_pairs={{0,1},{1,0},{2,3},{3,2},{4,5},{5,4},{6,7},{7,6},{8,9},{9,8},{10,11... | collective-permute-start | bytes 196616 | tf_op jit(solution)/shard_map/ppermute | solution.py:30
  142.2 6.3 %collective-permute-start.61 = (f32[64,256]{1,0:T(8,128)S(1)}, f32[64,256]{1,0:T(8,128)S(1)}, u32[]{:S(2)}, u32[]{:S(2)}) collective-permute-start(f32[64,256]{1,0:T(8,128)S(1)} %convolution_add_fusion.6), channel_id=1, source_target_pairs={{1,2},{2,1},{0,3},{3,0},{5,6},{6,5},{4,7},{7,4},{9,10},{10,9},{8,1... | collective-permute-start | bytes 196616 | tf_op jit(solution)/shard_map/ppermute | solution.py:31
  145.9 10.8 %collective-permute-start.59 = (f32[64,256]{1,0:T(8,128)S(1)}, f32[64,256]{1,0:T(8,128)S(1)}, u32[]{:S(2)}, u32[]{:S(2)}) collective-permute-start(f32[64,256]{1,0:T(8,128)S(1)} %collective-permute-done.57), channel_id=1, source_target_pairs={{1,0},{2,3},{5,4},{6,7},{9,8},{10,11},{13,12},{14,15},{17,16},{18,... | collective-permute-start | bytes 196616 | tf_op jit(solution)/shard_map/ppermute | solution.py:33
  147.2 9.5 %collective-permute-start.58 = (f32[64,256]{1,0:T(8,128)S(1)}, f32[64,256]{1,0:T(8,128)S(1)}, u32[]{:S(2)}, u32[]{:S(2)}) collective-permute-start(f32[64,256]{1,0:T(8,128)S(1)} %collective-permute-done.56), channel_id=1, source_target_pairs={{1,2},{2,1},{5,6},{6,5},{9,10},{10,9},{13,14},{14,13},{17,18},{18,... | collective-permute-start | bytes 196616 | tf_op jit(solution)/shard_map/ppermute | solution.py:32
  148.5 7.9 %collective-permute-start.63 = (f32[64,256]{1,0:T(8,128)S(1)}, f32[64,256]{1,0:T(8,128)S(1)}, u32[]{:S(2)}, u32[]{:S(2)}) collective-permute-start(f32[64,256]{1,0:T(8,128)S(1)} %collective-permute-done.61), channel_id=1, source_target_pairs={{1,0},{2,3},{5,4},{6,7},{9,8},{10,11},{13,12},{14,15},{17,16},{18,... | collective-permute-start | bytes 196616 | tf_op jit(solution)/shard_map/ppermute | solution.py:33
  149.8 6.6 %collective-permute-start.62 = (f32[64,256]{1,0:T(8,128)S(1)}, f32[64,256]{1,0:T(8,128)S(1)}, u32[]{:S(2)}, u32[]{:S(2)}) collective-permute-start(f32[64,256]{1,0:T(8,128)S(1)} %collective-permute-done.60), channel_id=1, source_target_pairs={{1,2},{2,1},{5,6},{6,5},{9,10},{10,9},{13,14},{14,13},{17,18},{18,... | collective-permute-start | bytes 196616 | tf_op jit(solution)/shard_map/ppermute | solution.py:32
  172.0 7.2 %collective-permute-start.68 = (f32[16,1280]{1,0:T(8,128)S(1)}, f32[16,1280]{1,0:T(8,128)S(1)}, u32[]{:S(2)}, u32[]{:S(2)}) collective-permute-start(f32[16,1280]{1,0:T(8,128)S(1)} %get-tuple-element.34), channel_id=1, source_target_pairs={{0,1},{1,2},{2,3},{3,0},{4,5},{5,6},{6,7},{7,4},{8,9},{9,10},{10,1... | collective-permute-start | bytes 245768 | tf_op jit(solution)/shard_map/ppermute | solution.py:21
  176.0 6.7 %collective-permute-start.69 = (f32[16,1280]{1,0:T(8,128)S(1)}, f32[16,1280]{1,0:T(8,128)S(1)}, u32[]{:S(2)}, u32[]{:S(2)}) collective-permute-start(f32[16,1280]{1,0:T(8,128)S(1)} %get-tuple-element.35), channel_id=1, source_target_pairs={{0,2},{1,3},{2,0},{3,1},{4,6},{5,7},{6,4},{7,5},{8,10},{9,11},{10,... | collective-permute-start | bytes 245768 | tf_op jit(solution)/shard_map/ppermute | solution.py:21
  176.3 6.3 %collective-permute-start.70 = (f32[16,1280]{1,0:T(8,128)S(1)}, f32[16,1280]{1,0:T(8,128)S(1)}, u32[]{:S(2)}, u32[]{:S(2)}) collective-permute-start(f32[16,1280]{1,0:T(8,128)S(1)} %get-tuple-element.36), channel_id=1, source_target_pairs={{0,3},{1,0},{2,1},{3,2},{4,7},{5,4},{6,5},{7,6},{8,11},{9,8},{10,9... | collective-permute-start | bytes 245768 | tf_op jit(solution)/shard_map/ppermute | solution.py:21
  184.4 5.6 %collective-permute-start.72 = (f32[16,256]{1,0:T(8,128)S(1)}, f32[16,256]{1,0:T(8,128)S(1)}, u32[]{:S(2)}, u32[]{:S(2)}) collective-permute-start(f32[16,256]{1,0:T(8,128)S(1)} %fusion.11), channel_id=1, source_target_pairs={{1,2},{2,1},{0,3},{3,0},{5,6},{6,5},{4,7},{7,4},{9,10},{10,9},{8,1... | collective-permute-start | bytes 49160 | tf_op jit(solution)/shard_map/ppermute | solution.py:31
  190.0 5.6 %collective-permute-start.74 = (f32[16,256]{1,0:T(8,128)S(1)}, f32[16,256]{1,0:T(8,128)S(1)}, u32[]{:S(2)}, u32[]{:S(2)}) collective-permute-start(f32[16,256]{1,0:T(8,128)S(1)} %collective-permute-done.72), channel_id=1, source_target_pairs={{1,0},{2,3},{5,4},{6,7},{9,8},{10,11},{13,12},{14,15},{17,16},{18,... | collective-permute-start | bytes 49160 | tf_op jit(solution)/shard_map/ppermute | solution.py:33
  195.8 8.9 %collective-permute-start.76 = (f32[16,256]{1,0:T(8,128)S(1)}, f32[16,256]{1,0:T(8,128)S(1)}, u32[]{:S(2)}, u32[]{:S(2)}) collective-permute-start(f32[16,256]{1,0:T(8,128)S(1)} %fusion.10), channel_id=1, source_target_pairs={{1,2},{2,1},{0,3},{3,0},{5,6},{6,5},{4,7},{7,4},{9,10},{10,9},{8,1... | collective-permute-start | bytes 49160 | tf_op jit(solution)/shard_map/ppermute | solution.py:31
  205.8 5.7 %collective-permute-start.78 = (f32[16,256]{1,0:T(8,128)S(1)}, f32[16,256]{1,0:T(8,128)S(1)}, u32[]{:S(2)}, u32[]{:S(2)}) collective-permute-start(f32[16,256]{1,0:T(8,128)S(1)} %collective-permute-done.76), channel_id=1, source_target_pairs={{1,0},{2,3},{5,4},{6,7},{9,8},{10,11},{13,12},{14,15},{17,16},{18,... | collective-permute-start | bytes 49160 | tf_op jit(solution)/shard_map/ppermute | solution.py:33
  (24 other events, 297.6 us)

commit v7 on v5

--- a/solution.py
+++ b/solution.py
@@ -16,9 +16,19 @@
     )
 
 
-def send(value, axis, shift):
+def partner(index, distance, count):
+    if count & (count - 1):
+        return lax.rem(index - distance + 2 * count, count)
+    return index ^ abs(distance)
+
+
+def send(value, axis, distance):
     count = lax.axis_size(axis)
-    return lax.ppermute(value, axis, [(i, (i + shift) % count) for i in range(count)])
+    if count & (count - 1):
+        pairs = [(i, (i + distance) % count) for i in range(count)]
+    else:
+        pairs = [(i, i ^ distance) for i in range(count)]
+    return lax.ppermute(value, axis, pairs)
 
 
 def gather_rows(value):
@@ -26,9 +36,9 @@
     me = lax.axis_index("grp")
     rows = value.shape[1]
     pieces = [(me * rows, value)]
-    for shift in range(1, members):
-        owner = lax.rem(me - shift + members, members)
-        pieces.append((owner * rows, send(value, "grp", shift)))
+    for distance in range(1, members):
+        owner = partner(me, distance, members)
+        pieces.append((owner * rows, send(value, "grp", distance)))
     return pieces
 
 
@@ -182,14 +192,14 @@
 
     first_share = share[:, 0]
     total = None
-    for shift in range(members):
-        target = lax.rem(me + shift, members)
+    for distance in range(members):
+        target = partner(me, -distance, members) if distance else me
         payload = [first_share] + [
             lax.dynamic_slice_in_dim(share[:, a], target * rows, rows, 1)
             for a in range(1, ancestors)
         ]
         payload = jnp.concatenate(payload, axis=1)
-        payload = payload if shift == 0 else send(payload, "grp", shift)
+        payload = send(payload, "grp", distance) if distance else payload
         total = payload if total is None else total + payload
     solutions = [contract_last(total[:, :order], diag_inv_anc[0])]
     for ancestor in range(1, ancestors):

time: 169 us -> 165 us (0.976)
  waiting for transfers between devices: 23.6 us -> 15.4 us
  starting transfers between devices: 86.2 us -> 89.6 us
    ppermute x57, waiting for transfers between devices: 20.6 us -> 11.9 us  [send(): return lax.ppermute(value, axis, pairs)]
    ppermute x57, starting transfers between devices: 82.6 us -> 85.3 us  [send(): return lax.ppermute(value, axis, pairs)]
  transfers between devices with their start and end apart: 61 -> 61, of which waited for: 17 -> 15; matrix products, arithmetic and copies ran while one was open for 24% -> 25% of each run, Pallas kernels for 0% -> 0%
where the time goes in v7:
time: 165 us; the launch traced here: 164 us
  starting transfers between devices  89.6 us (54%)
  matrix products  37 us (22%)
  waiting for transfers between devices  15.4 us (9%)
  local copies, waits for them, and re-layouts  12.1 us (7%)
  other arithmetic  7.1 us (4%)
  between operations  2.74 us (2%)
    ppermute x57, starting transfers between devices, send(): return lax.ppermute(value, axis, pairs)  85.3 us
    dot_general x79, matrix products, contract_last(): lax.dot_general(left, right, (((left.ndim - 1,), (right.ndim - 1,)), ((),...  36 us
    ppermute x57, waiting for transfers between devices, send(): return lax.ppermute(value, axis, pairs)  11.9 us
    unnamed x28, local copies, waits for them, and re-layouts  4.85 us
    ppermute x3, starting transfers between devices, swap(): return lax.ppermute(value, axis, pairs)  4.23 us
    ppermute x3, waiting for transfers between devices, swap(): return lax.ppermute(value, axis, pairs)  3.47 us
  transfers between devices with their start and end apart: 61, of which 15 were waited for; matrix products, arithmetic and copies ran while one was open for 25% of the time, Pallas kernels for 0%

profile of v7, /device:TPU:0, one launch (start us, length us, event | category | flops | bytes accessed | tf_op | source)
XLA Modules:
  0.0 164.0 jit_solution(16542799973163886423)
XLA Ops:
  0.6 2.2 %copy.28 = f32[1,4,256,128]{2,3,1,0:T(8,128)} copy(f32[1,4,256,128]{3,2,1,0:T(8,128)} %param.12) | data formatting | bytes 1048576 | tf_op args[0]
  2.8 1.5 slice_bitcast_fusion.20
  4.3 5.0 %collective-permute-start.5 = (f32[64,256]{1,0:T(8,128)}, f32[64,256]{1,0:T(8,128)}, u32[]{:S(2)}, u32[]{:S(2)}) collective-permute-start(f32[64,256]{1,0:T(8,128)} %get-tuple-element.21), channel_id=1, source_target_pairs={{0,3},{1,2},{2,1},{3,0},{4,7},{5,6},{6,5},{7,4},{8,11},{9,10},{10,... | collective-permute-start | bytes 196616 | tf_op jit(solution)/shard_map/ppermute | solution.py:31
  9.9 3.8 %collective-permute-start.2 = (f32[64,256]{1,0:T(8,128)S(1)}, f32[64,256]{1,0:T(8,128)S(1)}, u32[]{:S(2)}, u32[]{:S(2)}) collective-permute-start(f32[64,256]{1,0:T(8,128)S(1)} %get-tuple-element.20), channel_id=1, source_target_pairs={{0,3},{1,2},{2,1},{3,0},{4,7},{5,6},{6,5},{7,4},{8,11},{9,10},{10,... | collective-permute-start | bytes 196616 | tf_op jit(solution)/shard_map/ppermute | solution.py:31
  13.8 1.2 fusion.160
  15.0 1.2 fusion.162
  18.8 1.4 bitcast_dynamic-update-slice_fusion
  21.5 1.5 convolution_add_fusion.29
  23.1 1.2 fusion.152
  24.3 1.2 constant_dynamic-update-slice_fusion.3
  25.6 3.6 %collective-permute-start.14 = (f32[64,256]{1,0:T(8,128)S(1)}, f32[64,256]{1,0:T(8,128)S(1)}, u32[]{:S(2)}, u32[]{:S(2)}) collective-permute-start(f32[64,256]{1,0:T(8,128)S(1)} %bitcast.432), channel_id=1, source_target_pairs={{0,3},{1,2},{2,1},{3,0},{4,7},{5,6},{6,5},{7,4},{8,11},{9,10},{10,... | collective-permute-start | bytes 196616 | tf_op jit(solution)/shard_map/ppermute | solution.py:31
  30.0 1.2 convolution_add_fusion.31
  31.6 1.2 fusion.154
  32.9 1.2 constant_dynamic-update-slice_fusion.15
  34.4 3.6 %collective-permute-start.8 = (f32[64,256]{1,0:T(8,128)S(1)}, f32[64,256]{1,0:T(8,128)S(1)}, u32[]{:S(2)}, u32[]{:S(2)}) collective-permute-start(f32[64,256]{1,0:T(8,128)S(1)} %bitcast.436), channel_id=1, source_target_pairs={{0,3},{1,2},{2,1},{3,0},{4,7},{5,6},{6,5},{7,4},{8,11},{9,10},{10,... | collective-permute-start | bytes 196616 | tf_op jit(solution)/shard_map/ppermute | solution.py:31
  39.8 3.6 %collective-permute-start.17 = (f32[64,256]{1,0:T(8,128)S(1)}, f32[64,256]{1,0:T(8,128)S(1)}, u32[]{:S(2)}, u32[]{:S(2)}) collective-permute-start(f32[64,256]{1,0:T(8,128)S(1)} %fusion.16), channel_id=1, source_target_pairs={{0,3},{1,2},{2,1},{3,0},{4,7},{5,6},{6,5},{7,4},{8,11},{9,10},{10,... | collective-permute-start | bytes 196616 | tf_op jit(solution)/shard_map/ppermute | solution.py:31
  45.5 3.6 %collective-permute-start.11 = (f32[64,256]{1,0:T(8,128)S(1)}, f32[64,256]{1,0:T(8,128)S(1)}, u32[]{:S(2)}, u32[]{:S(2)}) collective-permute-start(f32[64,256]{1,0:T(8,128)S(1)} %fusion.19), channel_id=1, source_target_pairs={{0,3},{1,2},{2,1},{3,0},{4,7},{5,6},{6,5},{7,4},{8,11},{9,10},{10,... | collective-permute-start | bytes 196616 | tf_op jit(solution)/shard_map/ppermute | solution.py:31
  51.0 1.5 collective-permute-done.16
  52.9 2.0 %collective-permute-start.26 = (f32[64,256]{1,0:T(8,128)S(1)}, f32[64,256]{1,0:T(8,128)S(1)}, u32[]{:S(2)}, u32[]{:S(2)}) collective-permute-start(f32[64,256]{1,0:T(8,128)S(1)} %get-tuple-element.52), channel_id=1, source_target_pairs={{0,3},{1,2},{2,1},{3,0},{4,7},{5,6},{6,5},{7,4},{8,11},{9,10},{10,... | collective-permute-start | bytes 196616 | tf_op jit(solution)/shard_map/ppermute | solution.py:31
  55.3 2.4 %collective-permute-start.25 = (f32[64,256]{1,0:T(8,128)S(1)}, f32[64,256]{1,0:T(8,128)S(1)}, u32[]{:S(2)}, u32[]{:S(2)}) collective-permute-start(f32[64,256]{1,0:T(8,128)S(1)} %get-tuple-element.52), channel_id=1, source_target_pairs={{0,2},{1,3},{2,0},{3,1},{4,6},{5,7},{6,4},{7,5},{8,10},{9,11},{10,... | collective-permute-start | bytes 196616 | tf_op jit(solution)/shard_map/ppermute | solution.py:31
  58.6 2.0 %collective-permute-start.20 = (f32[64,256]{1,0:T(8,128)S(1)}, f32[64,256]{1,0:T(8,128)S(1)}, u32[]{:S(2)}, u32[]{:S(2)}) collective-permute-start(f32[64,256]{1,0:T(8,128)S(1)} %get-tuple-element.46), channel_id=1, source_target_pairs={{0,3},{1,2},{2,1},{3,0},{4,7},{5,6},{6,5},{7,4},{8,11},{9,10},{10,... | collective-permute-start | bytes 196616 | tf_op jit(solution)/shard_map/ppermute | solution.py:31
  61.1 2.4 %collective-permute-start.19 = (f32[64,256]{1,0:T(8,128)S(1)}, f32[64,256]{1,0:T(8,128)S(1)}, u32[]{:S(2)}, u32[]{:S(2)}) collective-permute-start(f32[64,256]{1,0:T(8,128)S(1)} %get-tuple-element.46), channel_id=1, source_target_pairs={{0,2},{1,3},{2,0},{3,1},{4,6},{5,7},{6,4},{7,5},{8,10},{9,11},{10,... | collective-permute-start | bytes 196616 | tf_op jit(solution)/shard_map/ppermute | solution.py:31
  64.4 2.0 %collective-permute-start.29 = (f32[64,256]{1,0:T(8,128)S(1)}, f32[64,256]{1,0:T(8,128)S(1)}, u32[]{:S(2)}, u32[]{:S(2)}) collective-permute-start(f32[64,256]{1,0:T(8,128)S(1)} %fusion.10), channel_id=1, source_target_pairs={{0,3},{1,2},{2,1},{3,0},{4,7},{5,6},{6,5},{7,4},{8,11},{9,10},{10,... | collective-permute-start | bytes 196616 | tf_op jit(solution)/shard_map/ppermute | solution.py:31
  66.8 2.4 %collective-permute-start.28 = (f32[64,256]{1,0:T(8,128)S(1)}, f32[64,256]{1,0:T(8,128)S(1)}, u32[]{:S(2)}, u32[]{:S(2)}) collective-permute-start(f32[64,256]{1,0:T(8,128)S(1)} %fusion.10), channel_id=1, source_target_pairs={{0,2},{1,3},{2,0},{3,1},{4,6},{5,7},{6,4},{7,5},{8,10},{9,11},{10,... | collective-permute-start | bytes 196616 | tf_op jit(solution)/shard_map/ppermute | solution.py:31
  70.1 2.0 %collective-permute-start.23 = (f32[64,256]{1,0:T(8,128)S(1)}, f32[64,256]{1,0:T(8,128)S(1)}, u32[]{:S(2)}, u32[]{:S(2)}) collective-permute-start(f32[64,256]{1,0:T(8,128)S(1)} %fusion.13), channel_id=1, source_target_pairs={{0,3},{1,2},{2,1},{3,0},{4,7},{5,6},{6,5},{7,4},{8,11},{9,10},{10,... | collective-permute-start | bytes 196616 | tf_op jit(solution)/shard_map/ppermute | solution.py:31
  72.6 2.5 %collective-permute-start.22 = (f32[64,256]{1,0:T(8,128)S(1)}, f32[64,256]{1,0:T(8,128)S(1)}, u32[]{:S(2)}, u32[]{:S(2)}) collective-permute-start(f32[64,256]{1,0:T(8,128)S(1)} %fusion.13), channel_id=1, source_target_pairs={{0,2},{1,3},{2,0},{3,1},{4,6},{5,7},{6,4},{7,5},{8,10},{9,11},{10,... | collective-permute-start | bytes 196616 | tf_op jit(solution)/shard_map/ppermute | solution.py:31
  76.0 2.0 %collective-permute-start.38 = (f32[64,256]{1,0:T(8,128)S(1)}, f32[64,256]{1,0:T(8,128)S(1)}, u32[]{:S(2)}, u32[]{:S(2)}) collective-permute-start(f32[64,256]{1,0:T(8,128)S(1)} %get-tuple-element.54), channel_id=1, source_target_pairs={{0,3},{1,2},{2,1},{3,0},{4,7},{5,6},{6,5},{7,4},{8,11},{9,10},{10,... | collective-permute-start | bytes 196616 | tf_op jit(solution)/shard_map/ppermute | solution.py:31
  78.4 2.4 %collective-permute-start.37 = (f32[64,256]{1,0:T(8,128)S(1)}, f32[64,256]{1,0:T(8,128)S(1)}, u32[]{:S(2)}, u32[]{:S(2)}) collective-permute-start(f32[64,256]{1,0:T(8,128)S(1)} %get-tuple-element.54), channel_id=1, source_target_pairs={{0,2},{1,3},{2,0},{3,1},{4,6},{5,7},{6,4},{7,5},{8,10},{9,11},{10,... | collective-permute-start | bytes 196616 | tf_op jit(solution)/shard_map/ppermute | solution.py:31
  81.7 2.0 %collective-permute-start.32 = (f32[64,256]{1,0:T(8,128)S(1)}, f32[64,256]{1,0:T(8,128)S(1)}, u32[]{:S(2)}, u32[]{:S(2)}) collective-permute-start(f32[64,256]{1,0:T(8,128)S(1)} %get-tuple-element.48), channel_id=1, source_target_pairs={{0,3},{1,2},{2,1},{3,0},{4,7},{5,6},{6,5},{7,4},{8,11},{9,10},{10,... | collective-permute-start | bytes 196616 | tf_op jit(solution)/shard_map/ppermute | solution.py:31
  84.1 2.4 %collective-permute-start.31 = (f32[64,256]{1,0:T(8,128)S(1)}, f32[64,256]{1,0:T(8,128)S(1)}, u32[]{:S(2)}, u32[]{:S(2)}) collective-permute-start(f32[64,256]{1,0:T(8,128)S(1)} %get-tuple-element.48), channel_id=1, source_target_pairs={{0,2},{1,3},{2,0},{3,1},{4,6},{5,7},{6,4},{7,5},{8,10},{9,11},{10,... | collective-permute-start | bytes 196616 | tf_op jit(solution)/shard_map/ppermute | solution.py:31
  87.4 2.0 %collective-permute-start.41 = (f32[64,256]{1,0:T(8,128)S(1)}, f32[64,256]{1,0:T(8,128)S(1)}, u32[]{:S(2)}, u32[]{:S(2)}) collective-permute-start(f32[64,256]{1,0:T(8,128)S(1)} %fusion.4), channel_id=1, source_target_pairs={{0,3},{1,2},{2,1},{3,0},{4,7},{5,6},{6,5},{7,4},{8,11},{9,10},{10,... | collective-permute-start | bytes 196616 | tf_op jit(solution)/shard_map/ppermute | solution.py:31
  90.3 2.0 %collective-permute-start.40 = (f32[64,256]{1,0:T(8,128)S(1)}, f32[64,256]{1,0:T(8,128)S(1)}, u32[]{:S(2)}, u32[]{:S(2)}) collective-permute-start(f32[64,256]{1,0:T(8,128)S(1)} %fusion.4), channel_id=1, source_target_pairs={{0,2},{1,3},{2,0},{3,1},{4,6},{5,7},{6,4},{7,5},{8,10},{9,11},{10,... | collective-permute-start | bytes 196616 | tf_op jit(solution)/shard_map/ppermute | solution.py:31
  93.1 2.0 %collective-permute-start.35 = (f32[64,256]{1,0:T(8,128)S(1)}, f32[64,256]{1,0:T(8,128)S(1)}, u32[]{:S(2)}, u32[]{:S(2)}) collective-permute-start(f32[64,256]{1,0:T(8,128)S(1)} %fusion.7), channel_id=1, source_target_pairs={{0,3},{1,2},{2,1},{3,0},{4,7},{5,6},{6,5},{7,4},{8,11},{9,10},{10,... | collective-permute-start | bytes 196616 | tf_op jit(solution)/shard_map/ppermute | solution.py:31
  98.7 2.5 %collective-permute-start.34 = (f32[64,256]{1,0:T(8,128)S(1)}, f32[64,256]{1,0:T(8,128)S(1)}, u32[]{:S(2)}, u32[]{:S(2)}) collective-permute-start(f32[64,256]{1,0:T(8,128)S(1)} %fusion.7), channel_id=1, source_target_pairs={{0,2},{1,3},{2,0},{3,1},{4,6},{5,7},{6,4},{7,5},{8,10},{9,11},{10,... | collective-permute-start | bytes 196616 | tf_op jit(solution)/shard_map/ppermute | solution.py:31
  102.0 2.0 %collective-permute-start.47 = (f32[64,256]{1,0:T(8,128)S(1)}, f32[64,256]{1,0:T(8,128)S(1)}, u32[]{:S(2)}, u32[]{:S(2)}) collective-permute-start(f32[64,256]{1,0:T(8,128)S(1)} %fusion.2), channel_id=1, source_target_pairs={{0,3},{1,2},{2,1},{3,0},{4,7},{5,6},{6,5},{7,4},{8,11},{9,10},{10,... | collective-permute-start | bytes 196616 | tf_op jit(solution)/shard_map/ppermute | solution.py:31
  104.1 2.4 %collective-permute-start.46 = (f32[64,256]{1,0:T(8,128)S(1)}, f32[64,256]{1,0:T(8,128)S(1)}, u32[]{:S(2)}, u32[]{:S(2)}) collective-permute-start(f32[64,256]{1,0:T(8,128)S(1)} %fusion.2), channel_id=1, source_target_pairs={{0,2},{1,3},{2,0},{3,1},{4,6},{5,7},{6,4},{7,5},{8,10},{9,11},{10,... | collective-permute-start | bytes 196616 | tf_op jit(solution)/shard_map/ppermute | solution.py:31
  107.7 2.0 %collective-permute-start.44 = (f32[64,256]{1,0:T(8,128)S(1)}, f32[64,256]{1,0:T(8,128)S(1)}, u32[]{:S(2)}, u32[]{:S(2)}) collective-permute-start(f32[64,256]{1,0:T(8,128)S(1)} %fusion.5), channel_id=1, source_target_pairs={{0,3},{1,2},{2,1},{3,0},{4,7},{5,6},{6,5},{7,4},{8,11},{9,10},{10,... | collective-permute-start | bytes 196616 | tf_op jit(solution)/shard_map/ppermute | solution.py:31
  110.2 2.4 %collective-permute-start.43 = (f32[64,256]{1,0:T(8,128)S(1)}, f32[64,256]{1,0:T(8,128)S(1)}, u32[]{:S(2)}, u32[]{:S(2)}) collective-permute-start(f32[64,256]{1,0:T(8,128)S(1)} %fusion.5), channel_id=1, source_target_pairs={{0,2},{1,3},{2,0},{3,1},{4,6},{5,7},{6,4},{7,5},{8,10},{9,11},{10,... | collective-permute-start | bytes 196616 | tf_op jit(solution)/shard_map/ppermute | solution.py:31
  113.6 1.0 collective-permute-done.42
  117.3 3.6 %collective-permute-start.51 = (f32[2,16,512]{2,1,0:T(8,128)S(1)}, f32[2,16,512]{2,1,0:T(8,128)S(1)}, u32[]{:S(2)}, u32[]{:S(2)}) collective-permute-start(f32[2,16,512]{2,1,0:T(8,128)S(1)} %get-tuple-element.25), channel_id=1, source_target_pairs={{0,24},{4,28},{8,16},{12,20},{16,8},{20,12},{24,0},{28,4},{1,25},{... | collective-permute-start | bytes 196616 | tf_op jit(solution)/shard_map/ppermute | solution.py:74
  122.2 1.4 collective-permute-done.51
  123.6 1.5 collective-permute-done.50
  127.0 1.0 reshape.397
  128.8 1.0 convolution_bitcast_fusion
  129.8 1.0 reshape.398
  130.8 1.1 copy_subtract_fusion
  132.0 1.4 collective-permute-start.54
  133.3 1.0 collective-permute-start.53
  134.3 2.1 %collective-permute-start.52 = (f32[16,1280]{1,0:T(8,128)S(1)}, f32[16,1280]{1,0:T(8,128)S(1)}, u32[]{:S(2)}, u32[]{:S(2)}) collective-permute-start(f32[16,1280]{1,0:T(8,128)S(1)} %get-tuple-element.34), channel_id=1, source_target_pairs={{0,1},{1,0},{2,3},{3,2},{4,5},{5,4},{6,7},{7,6},{8,9},{9,8},{10,11... | collective-permute-start | bytes 245768 | tf_op jit(solution)/shard_map/ppermute | solution.py:31
  136.4 2.6 %collective-permute-done.54 = f32[16,1280]{1,0:T(8,128)S(1)} collective-permute-done((f32[16,1280]{1,0:T(8,128)S(1)}, f32[16,1280]{1,0:T(8,128)S(1)}, u32[]{:S(2)}, u32[]{:S(2)}) %collective-permute-start.54) | collective-permute-done | bytes 81952 | tf_op jit(solution)/shard_map/ppermute | solution.py:31
  139.0 2.6 %collective-permute-done.53 = f32[16,1280]{1,0:T(8,128)S(1)} collective-permute-done((f32[16,1280]{1,0:T(8,128)S(1)}, f32[16,1280]{1,0:T(8,128)S(1)}, u32[]{:S(2)}, u32[]{:S(2)}) %collective-permute-start.53) | collective-permute-done | bytes 81952 | tf_op jit(solution)/shard_map/ppermute | solution.py:31
  141.6 1.7 %fusion.26 = f32[16,256]{1,0:T(8,128)S(1)} fusion(f32[2,256,1024]{2,1,0:T(8,128)} %param.20, f32[16,1280]{1,0:T(8,128)S(1)} %fusion.231), kind=kOutput, calls=%fused_computation.62 | convolution fusion | flops 25165824 | bytes 1130496 | tf_op jit(solution)/shard_map/dot_general | solution.py:10
  143.4 1.8 %collective-permute-start.57 = (f32[16,256]{1,0:T(8,128)S(1)}, f32[16,256]{1,0:T(8,128)S(1)}, u32[]{:S(2)}, u32[]{:S(2)}) collective-permute-start(f32[16,256]{1,0:T(8,128)S(1)} %fusion.26), channel_id=1, source_target_pairs={{0,3},{1,2},{2,1},{3,0},{4,7},{5,6},{6,5},{7,4},{8,11},{9,10},{10,... | collective-permute-start | bytes 49160 | tf_op jit(solution)/shard_map/ppermute | solution.py:31
  145.2 2.6 %collective-permute-start.56 = (f32[16,256]{1,0:T(8,128)S(1)}, f32[16,256]{1,0:T(8,128)S(1)}, u32[]{:S(2)}, u32[]{:S(2)}) collective-permute-start(f32[16,256]{1,0:T(8,128)S(1)} %fusion.26), channel_id=1, source_target_pairs={{0,2},{1,3},{2,0},{3,1},{4,6},{5,7},{6,4},{7,5},{8,10},{9,11},{10,... | collective-permute-start | bytes 49160 | tf_op jit(solution)/shard_map/ppermute | solution.py:31
  148.0 1.1 collective-permute-done.55
  150.1 2.2 %collective-permute-start.60 = (f32[16,256]{1,0:T(8,128)S(1)}, f32[16,256]{1,0:T(8,128)S(1)}, u32[]{:S(2)}, u32[]{:S(2)}) collective-permute-start(f32[16,256]{1,0:T(8,128)S(1)} %slice_subtract_fusion), channel_id=1, source_target_pairs={{0,3},{1,2},{2,1},{3,0},{4,7},{5,6},{6,5},{7,4},{8,11},{9,10},{10,... | collective-permute-start | bytes 49160 | tf_op jit(solution)/shard_map/ppermute | solution.py:31
  153.1 2.0 %copy.32 = f32[1,4,256,128]{3,2,1,0:T(8,128)} copy(f32[1,4,256,128]{2,3,1,0:T(8,128)} %maximum_bitcast_fusion) | data formatting | bytes 1048576
  155.1 1.4 collective-permute-start.59
  156.5 0.9 collective-permute-start.58
  157.4 1.1 fusion.67
  158.6 1.2 collective-permute-done.59
  159.7 1.1 fusion.69
  160.9 1.1 fusion.71
  162.1 1.2 fusion.24
  (221 shorter events, 36.5 us)
Async XLA Ops:
  0.6 30.6 %copy-start = (f32[1,3,256,1024]{3,2,1,0:T(8,128)S(1)}, f32[1,3,256,1024]{3,2,1,0:T(8,128)}, u32[]{:S(2)}) copy-start(f32[1,3,256,1024]{3,2,1,0:T(8,128)} %param.14) | copy-start | bytes 9437188
  4.3 18.7 %collective-permute-start.5 = (f32[64,256]{1,0:T(8,128)}, f32[64,256]{1,0:T(8,128)}, u32[]{:S(2)}, u32[]{:S(2)}) collective-permute-start(f32[64,256]{1,0:T(8,128)} %get-tuple-element.21), channel_id=1, source_target_pairs={{0,3},{1,2},{2,1},{3,0},{4,7},{5,6},{6,5},{7,4},{8,11},{9,10},{10,... | collective-permute-start | bytes 196616 | tf_op jit(solution)/shard_map/ppermute | solution.py:31
  9.4 11.5 %collective-permute-start.3 = (f32[64,256]{1,0:T(8,128)}, f32[64,256]{1,0:T(8,128)}, u32[]{:S(2)}, u32[]{:S(2)}) collective-permute-start(f32[64,256]{1,0:T(8,128)} %get-tuple-element.21), channel_id=1, source_target_pairs={{0,1},{1,0},{2,3},{3,2},{4,5},{5,4},{6,7},{7,6},{8,9},{9,8},{10,11... | collective-permute-start | bytes 196616 | tf_op jit(solution)/shard_map/ppermute | solution.py:31
  9.4 14.9 %collective-permute-start.4 = (f32[64,256]{1,0:T(8,128)}, f32[64,256]{1,0:T(8,128)S(1)}, u32[]{:S(2)}, u32[]{:S(2)}) collective-permute-start(f32[64,256]{1,0:T(8,128)} %get-tuple-element.21), channel_id=1, source_target_pairs={{0,2},{1,3},{2,0},{3,1},{4,6},{5,7},{6,4},{7,5},{8,10},{9,11},{10,... | collective-permute-start | bytes 196616 | tf_op jit(solution)/shard_map/ppermute | solution.py:31
  9.9 21.6 %collective-permute-start.2 = (f32[64,256]{1,0:T(8,128)S(1)}, f32[64,256]{1,0:T(8,128)S(1)}, u32[]{:S(2)}, u32[]{:S(2)}) collective-permute-start(f32[64,256]{1,0:T(8,128)S(1)} %get-tuple-element.20), channel_id=1, source_target_pairs={{0,3},{1,2},{2,1},{3,0},{4,7},{5,6},{6,5},{7,4},{8,11},{9,10},{10,... | collective-permute-start | bytes 196616 | tf_op jit(solution)/shard_map/ppermute | solution.py:31
  13.8 15.4 %collective-permute-start = (f32[64,256]{1,0:T(8,128)S(1)}, f32[64,256]{1,0:T(8,128)S(1)}, u32[]{:S(2)}, u32[]{:S(2)}) collective-permute-start(f32[64,256]{1,0:T(8,128)S(1)} %get-tuple-element.20), channel_id=1, source_target_pairs={{0,1},{1,0},{2,3},{3,2},{4,5},{5,4},{6,7},{7,6},{8,9},{9,8},{10,11... | collective-permute-start | bytes 196616 | tf_op jit(solution)/shard_map/ppermute | solution.py:31
  20.9 22.4 %copy-start.2 = (f32[1,4,256,1024]{3,2,1,0:T(8,128)S(1)}, f32[1,4,256,1024]{3,2,1,0:T(8,128)}, u32[]{:S(2)}) copy-start(f32[1,4,256,1024]{3,2,1,0:T(8,128)} %param.13) | copy-start | bytes 12582916
  20.9 11.9 %collective-permute-start.1 = (f32[64,256]{1,0:T(8,128)S(1)}, f32[64,256]{1,0:T(8,128)S(1)}, u32[]{:S(2)}, u32[]{:S(2)}) collective-permute-start(f32[64,256]{1,0:T(8,128)S(1)} %get-tuple-element.20), channel_id=1, source_target_pairs={{0,2},{1,3},{2,0},{3,1},{4,6},{5,7},{6,4},{7,5},{8,10},{9,11},{10,... | collective-permute-start | bytes 196616 | tf_op jit(solution)/shard_map/ppermute | solution.py:31
  25.6 13.5 %collective-permute-start.14 = (f32[64,256]{1,0:T(8,128)S(1)}, f32[64,256]{1,0:T(8,128)S(1)}, u32[]{:S(2)}, u32[]{:S(2)}) collective-permute-start(f32[64,256]{1,0:T(8,128)S(1)} %bitcast.432), channel_id=1, source_target_pairs={{0,3},{1,2},{2,1},{3,0},{4,7},{5,6},{6,5},{7,4},{8,11},{9,10},{10,... | collective-permute-start | bytes 196616 | tf_op jit(solution)/shard_map/ppermute | solution.py:31
  29.2 8.8 %collective-permute-start.12 = (f32[64,256]{1,0:T(8,128)S(1)}, f32[64,256]{1,0:T(8,128)S(1)}, u32[]{:S(2)}, u32[]{:S(2)}) collective-permute-start(f32[64,256]{1,0:T(8,128)S(1)} %bitcast.433), channel_id=1, source_target_pairs={{0,1},{1,0},{2,3},{3,2},{4,5},{5,4},{6,7},{7,6},{8,9},{9,8},{10,11... | collective-permute-start | bytes 196616 | tf_op jit(solution)/shard_map/ppermute | solution.py:31
  29.2 10.3 %collective-permute-start.13 = (f32[64,256]{1,0:T(8,128)S(1)}, f32[64,256]{1,0:T(8,128)S(1)}, u32[]{:S(2)}, u32[]{:S(2)}) collective-permute-start(f32[64,256]{1,0:T(8,128)S(1)} %bitcast.434), channel_id=1, source_target_pairs={{0,2},{1,3},{2,0},{3,1},{4,6},{5,7},{6,4},{7,5},{8,10},{9,11},{10,... | collective-permute-start | bytes 196616 | tf_op jit(solution)/shard_map/ppermute | solution.py:31
  34.4 10.5 %collective-permute-start.8 = (f32[64,256]{1,0:T(8,128)S(1)}, f32[64,256]{1,0:T(8,128)S(1)}, u32[]{:S(2)}, u32[]{:S(2)}) collective-permute-start(f32[64,256]{1,0:T(8,128)S(1)} %bitcast.436), channel_id=1, source_target_pairs={{0,3},{1,2},{2,1},{3,0},{4,7},{5,6},{6,5},{7,4},{8,11},{9,10},{10,... | collective-permute-start | bytes 196616 | tf_op jit(solution)/shard_map/ppermute | solution.py:31
  38.0 6.1 %collective-permute-start.6 = (f32[64,256]{1,0:T(8,128)S(1)}, f32[64,256]{1,0:T(8,128)S(1)}, u32[]{:S(2)}, u32[]{:S(2)}) collective-permute-start(f32[64,256]{1,0:T(8,128)S(1)} %bitcast.437), channel_id=1, source_target_pairs={{0,1},{1,0},{2,3},{3,2},{4,5},{5,4},{6,7},{7,6},{8,9},{9,8},{10,11... | collective-permute-start | bytes 196616 | tf_op jit(solution)/shard_map/ppermute | solution.py:31
  38.0 7.2 %collective-permute-start.7 = (f32[64,256]{1,0:T(8,128)S(1)}, f32[64,256]{1,0:T(8,128)S(1)}, u32[]{:S(2)}, u32[]{:S(2)}) collective-permute-start(f32[64,256]{1,0:T(8,128)S(1)} %bitcast.438), channel_id=1, source_target_pairs={{0,2},{1,3},{2,0},{3,1},{4,6},{5,7},{6,4},{7,5},{8,10},{9,11},{10,... | collective-permute-start | bytes 196616 | tf_op jit(solution)/shard_map/ppermute | solution.py:31
  39.8 11.0 %collective-permute-start.17 = (f32[64,256]{1,0:T(8,128)S(1)}, f32[64,256]{1,0:T(8,128)S(1)}, u32[]{:S(2)}, u32[]{:S(2)}) collective-permute-start(f32[64,256]{1,0:T(8,128)S(1)} %fusion.16), channel_id=1, source_target_pairs={{0,3},{1,2},{2,1},{3,0},{4,7},{5,6},{6,5},{7,4},{8,11},{9,10},{10,... | collective-permute-start | bytes 196616 | tf_op jit(solution)/shard_map/ppermute | solution.py:31
  43.6 6.3 %collective-permute-start.15 = (f32[64,256]{1,0:T(8,128)S(1)}, f32[64,256]{1,0:T(8,128)S(1)}, u32[]{:S(2)}, u32[]{:S(2)}) collective-permute-start(f32[64,256]{1,0:T(8,128)S(1)} %fusion.16), channel_id=1, source_target_pairs={{0,1},{1,0},{2,3},{3,2},{4,5},{5,4},{6,7},{7,6},{8,9},{9,8},{10,11... | collective-permute-start | bytes 196616 | tf_op jit(solution)/shard_map/ppermute | solution.py:31
  44.1 8.5 %collective-permute-start.16 = (f32[64,256]{1,0:T(8,128)S(1)}, f32[64,256]{1,0:T(8,128)S(1)}, u32[]{:S(2)}, u32[]{:S(2)}) collective-permute-start(f32[64,256]{1,0:T(8,128)S(1)} %fusion.16), channel_id=1, source_target_pairs={{0,2},{1,3},{2,0},{3,1},{4,6},{5,7},{6,4},{7,5},{8,10},{9,11},{10,... | collective-permute-start | bytes 196616 | tf_op jit(solution)/shard_map/ppermute | solution.py:31
  45.5 12.5 %collective-permute-start.11 = (f32[64,256]{1,0:T(8,128)S(1)}, f32[64,256]{1,0:T(8,128)S(1)}, u32[]{:S(2)}, u32[]{:S(2)}) collective-permute-start(f32[64,256]{1,0:T(8,128)S(1)} %fusion.19), channel_id=1, source_target_pairs={{0,3},{1,2},{2,1},{3,0},{4,7},{5,6},{6,5},{7,4},{8,11},{9,10},{10,... | collective-permute-start | bytes 196616 | tf_op jit(solution)/shard_map/ppermute | solution.py:31
  49.3 6.0 %collective-permute-start.9 = (f32[64,256]{1,0:T(8,128)S(1)}, f32[64,256]{1,0:T(8,128)S(1)}, u32[]{:S(2)}, u32[]{:S(2)}) collective-permute-start(f32[64,256]{1,0:T(8,128)S(1)} %fusion.19), channel_id=1, source_target_pairs={{0,1},{1,0},{2,3},{3,2},{4,5},{5,4},{6,7},{7,6},{8,9},{9,8},{10,11... | collective-permute-start | bytes 196616 | tf_op jit(solution)/shard_map/ppermute | solution.py:31
  49.9 8.4 %collective-permute-start.10 = (f32[64,256]{1,0:T(8,128)S(1)}, f32[64,256]{1,0:T(8,128)S(1)}, u32[]{:S(2)}, u32[]{:S(2)}) collective-permute-start(f32[64,256]{1,0:T(8,128)S(1)} %fusion.19), channel_id=1, source_target_pairs={{0,2},{1,3},{2,0},{3,1},{4,6},{5,7},{6,4},{7,5},{8,10},{9,11},{10,... | collective-permute-start | bytes 196616 | tf_op jit(solution)/shard_map/ppermute | solution.py:31
  52.9 10.8 %collective-permute-start.26 = (f32[64,256]{1,0:T(8,128)S(1)}, f32[64,256]{1,0:T(8,128)S(1)}, u32[]{:S(2)}, u32[]{:S(2)}) collective-permute-start(f32[64,256]{1,0:T(8,128)S(1)} %get-tuple-element.52), channel_id=1, source_target_pairs={{0,3},{1,2},{2,1},{3,0},{4,7},{5,6},{6,5},{7,4},{8,11},{9,10},{10,... | collective-permute-start | bytes 196616 | tf_op jit(solution)/shard_map/ppermute | solution.py:31
  55.2 5.8 %collective-permute-start.24 = (f32[64,256]{1,0:T(8,128)S(1)}, f32[64,256]{1,0:T(8,128)S(1)}, u32[]{:S(2)}, u32[]{:S(2)}) collective-permute-start(f32[64,256]{1,0:T(8,128)S(1)} %get-tuple-element.52), channel_id=1, source_target_pairs={{0,1},{1,0},{2,3},{3,2},{4,5},{5,4},{6,7},{7,6},{8,9},{9,8},{10,11... | collective-permute-start | bytes 196616 | tf_op jit(solution)/shard_map/ppermute | solution.py:31
  55.3 8.7 %collective-permute-start.25 = (f32[64,256]{1,0:T(8,128)S(1)}, f32[64,256]{1,0:T(8,128)S(1)}, u32[]{:S(2)}, u32[]{:S(2)}) collective-permute-start(f32[64,256]{1,0:T(8,128)S(1)} %get-tuple-element.52), channel_id=1, source_target_pairs={{0,2},{1,3},{2,0},{3,1},{4,6},{5,7},{6,4},{7,5},{8,10},{9,11},{10,... | collective-permute-start | bytes 196616 | tf_op jit(solution)/shard_map/ppermute | solution.py:31
  58.6 10.8 %collective-permute-start.20 = (f32[64,256]{1,0:T(8,128)S(1)}, f32[64,256]{1,0:T(8,128)S(1)}, u32[]{:S(2)}, u32[]{:S(2)}) collective-permute-start(f32[64,256]{1,0:T(8,128)S(1)} %get-tuple-element.46), channel_id=1, source_target_pairs={{0,3},{1,2},{2,1},{3,0},{4,7},{5,6},{6,5},{7,4},{8,11},{9,10},{10,... | collective-permute-start | bytes 196616 | tf_op jit(solution)/shard_map/ppermute | solution.py:31
  61.0 5.8 %collective-permute-start.18 = (f32[64,256]{1,0:T(8,128)S(1)}, f32[64,256]{1,0:T(8,128)S(1)}, u32[]{:S(2)}, u32[]{:S(2)}) collective-permute-start(f32[64,256]{1,0:T(8,128)S(1)} %get-tuple-element.46), channel_id=1, source_target_pairs={{0,1},{1,0},{2,3},{3,2},{4,5},{5,4},{6,7},{7,6},{8,9},{9,8},{10,11... | collective-permute-start | bytes 196616 | tf_op jit(solution)/shard_map/ppermute | solution.py:31
  61.1 8.7 %collective-permute-start.19 = (f32[64,256]{1,0:T(8,128)S(1)}, f32[64,256]{1,0:T(8,128)S(1)}, u32[]{:S(2)}, u32[]{:S(2)}) collective-permute-start(f32[64,256]{1,0:T(8,128)S(1)} %get-tuple-element.46), channel_id=1, source_target_pairs={{0,2},{1,3},{2,0},{3,1},{4,6},{5,7},{6,4},{7,5},{8,10},{9,11},{10,... | collective-permute-start | bytes 196616 | tf_op jit(solution)/shard_map/ppermute | solution.py:31
  64.4 11.0 %collective-permute-start.29 = (f32[64,256]{1,0:T(8,128)S(1)}, f32[64,256]{1,0:T(8,128)S(1)}, u32[]{:S(2)}, u32[]{:S(2)}) collective-permute-start(f32[64,256]{1,0:T(8,128)S(1)} %fusion.10), channel_id=1, source_target_pairs={{0,3},{1,2},{2,1},{3,0},{4,7},{5,6},{6,5},{7,4},{8,11},{9,10},{10,... | collective-permute-start | bytes 196616 | tf_op jit(solution)/shard_map/ppermute | solution.py:31
  66.7 5.9 %collective-permute-start.27 = (f32[64,256]{1,0:T(8,128)S(1)}, f32[64,256]{1,0:T(8,128)S(1)}, u32[]{:S(2)}, u32[]{:S(2)}) collective-permute-start(f32[64,256]{1,0:T(8,128)S(1)} %fusion.10), channel_id=1, source_target_pairs={{0,1},{1,0},{2,3},{3,2},{4,5},{5,4},{6,7},{7,6},{8,9},{9,8},{10,11... | collective-permute-start | bytes 196616 | tf_op jit(solution)/shard_map/ppermute | solution.py:31
  66.8 8.9 %collective-permute-start.28 = (f32[64,256]{1,0:T(8,128)S(1)}, f32[64,256]{1,0:T(8,128)S(1)}, u32[]{:S(2)}, u32[]{:S(2)}) collective-permute-start(f32[64,256]{1,0:T(8,128)S(1)} %fusion.10), channel_id=1, source_target_pairs={{0,2},{1,3},{2,0},{3,1},{4,6},{5,7},{6,4},{7,5},{8,10},{9,11},{10,... | collective-permute-start | bytes 196616 | tf_op jit(solution)/shard_map/ppermute | solution.py:31
  70.1 11.0 %collective-permute-start.23 = (f32[64,256]{1,0:T(8,128)S(1)}, f32[64,256]{1,0:T(8,128)S(1)}, u32[]{:S(2)}, u32[]{:S(2)}) collective-permute-start(f32[64,256]{1,0:T(8,128)S(1)} %fusion.13), channel_id=1, source_target_pairs={{0,3},{1,2},{2,1},{3,0},{4,7},{5,6},{6,5},{7,4},{8,11},{9,10},{10,... | collective-permute-start | bytes 196616 | tf_op jit(solution)/shard_map/ppermute | solution.py:31
  72.4 6.0 %collective-permute-start.21 = (f32[64,256]{1,0:T(8,128)S(1)}, f32[64,256]{1,0:T(8,128)S(1)}, u32[]{:S(2)}, u32[]{:S(2)}) collective-permute-start(f32[64,256]{1,0:T(8,128)S(1)} %fusion.13), channel_id=1, source_target_pairs={{0,1},{1,0},{2,3},{3,2},{4,5},{5,4},{6,7},{7,6},{8,9},{9,8},{10,11... | collective-permute-start | bytes 196616 | tf_op jit(solution)/shard_map/ppermute | solution.py:31
  72.6 8.8 %collective-permute-start.22 = (f32[64,256]{1,0:T(8,128)S(1)}, f32[64,256]{1,0:T(8,128)S(1)}, u32[]{:S(2)}, u32[]{:S(2)}) collective-permute-start(f32[64,256]{1,0:T(8,128)S(1)} %fusion.13), channel_id=1, source_target_pairs={{0,2},{1,3},{2,0},{3,1},{4,6},{5,7},{6,4},{7,5},{8,10},{9,11},{10,... | collective-permute-start | bytes 196616 | tf_op jit(solution)/shard_map/ppermute | solution.py:31
  76.0 10.8 %collective-permute-start.38 = (f32[64,256]{1,0:T(8,128)S(1)}, f32[64,256]{1,0:T(8,128)S(1)}, u32[]{:S(2)}, u32[]{:S(2)}) collective-permute-start(f32[64,256]{1,0:T(8,128)S(1)} %get-tuple-element.54), channel_id=1, source_target_pairs={{0,3},{1,2},{2,1},{3,0},{4,7},{5,6},{6,5},{7,4},{8,11},{9,10},{10,... | collective-permute-start | bytes 196616 | tf_op jit(solution)/shard_map/ppermute | solution.py:31
  78.3 5.8 %collective-permute-start.36 = (f32[64,256]{1,0:T(8,128)S(1)}, f32[64,256]{1,0:T(8,128)S(1)}, u32[]{:S(2)}, u32[]{:S(2)}) collective-permute-start(f32[64,256]{1,0:T(8,128)S(1)} %get-tuple-element.54), channel_id=1, source_target_pairs={{0,1},{1,0},{2,3},{3,2},{4,5},{5,4},{6,7},{7,6},{8,9},{9,8},{10,11... | collective-permute-start | bytes 196616 | tf_op jit(solution)/shard_map/ppermute | solution.py:31
  78.4 8.7 %collective-permute-start.37 = (f32[64,256]{1,0:T(8,128)S(1)}, f32[64,256]{1,0:T(8,128)S(1)}, u32[]{:S(2)}, u32[]{:S(2)}) collective-permute-start(f32[64,256]{1,0:T(8,128)S(1)} %get-tuple-element.54), channel_id=1, source_target_pairs={{0,2},{1,3},{2,0},{3,1},{4,6},{5,7},{6,4},{7,5},{8,10},{9,11},{10,... | collective-permute-start | bytes 196616 | tf_op jit(solution)/shard_map/ppermute | solution.py:31
  81.7 10.8 %collective-permute-start.32 = (f32[64,256]{1,0:T(8,128)S(1)}, f32[64,256]{1,0:T(8,128)S(1)}, u32[]{:S(2)}, u32[]{:S(2)}) collective-permute-start(f32[64,256]{1,0:T(8,128)S(1)} %get-tuple-element.48), channel_id=1, source_target_pairs={{0,3},{1,2},{2,1},{3,0},{4,7},{5,6},{6,5},{7,4},{8,11},{9,10},{10,... | collective-permute-start | bytes 196616 | tf_op jit(solution)/shard_map/ppermute | solution.py:31
  84.0 6.2 %collective-permute-start.30 = (f32[64,256]{1,0:T(8,128)S(1)}, f32[64,256]{1,0:T(8,128)S(1)}, u32[]{:S(2)}, u32[]{:S(2)}) collective-permute-start(f32[64,256]{1,0:T(8,128)S(1)} %get-tuple-element.48), channel_id=1, source_target_pairs={{0,1},{1,0},{2,3},{3,2},{4,5},{5,4},{6,7},{7,6},{8,9},{9,8},{10,11... | collective-permute-start | bytes 196616 | tf_op jit(solution)/shard_map/ppermute | solution.py:31
  84.1 8.7 %collective-permute-start.31 = (f32[64,256]{1,0:T(8,128)S(1)}, f32[64,256]{1,0:T(8,128)S(1)}, u32[]{:S(2)}, u32[]{:S(2)}) collective-permute-start(f32[64,256]{1,0:T(8,128)S(1)} %get-tuple-element.48), channel_id=1, source_target_pairs={{0,2},{1,3},{2,0},{3,1},{4,6},{5,7},{6,4},{7,5},{8,10},{9,11},{10,... | collective-permute-start | bytes 196616 | tf_op jit(solution)/shard_map/ppermute | solution.py:31
  87.4 14.0 %collective-permute-start.41 = (f32[64,256]{1,0:T(8,128)S(1)}, f32[64,256]{1,0:T(8,128)S(1)}, u32[]{:S(2)}, u32[]{:S(2)}) collective-permute-start(f32[64,256]{1,0:T(8,128)S(1)} %fusion.4), channel_id=1, source_target_pairs={{0,3},{1,2},{2,1},{3,0},{4,7},{5,6},{6,5},{7,4},{8,11},{9,10},{10,... | collective-permute-start | bytes 196616 | tf_op jit(solution)/shard_map/ppermute | solution.py:31
  89.8 8.9 %collective-permute-start.39 = (f32[64,256]{1,0:T(8,128)S(1)}, f32[64,256]{1,0:T(8,128)S(1)}, u32[]{:S(2)}, u32[]{:S(2)}) collective-permute-start(f32[64,256]{1,0:T(8,128)S(1)} %fusion.4), channel_id=1, source_target_pairs={{0,1},{1,0},{2,3},{3,2},{4,5},{5,4},{6,7},{7,6},{8,9},{9,8},{10,11... | collective-permute-start | bytes 196616 | tf_op jit(solution)/shard_map/ppermute | solution.py:31
  90.3 11.5 %collective-permute-start.40 = (f32[64,256]{1,0:T(8,128)S(1)}, f32[64,256]{1,0:T(8,128)S(1)}, u32[]{:S(2)}, u32[]{:S(2)}) collective-permute-start(f32[64,256]{1,0:T(8,128)S(1)} %fusion.4), channel_id=1, source_target_pairs={{0,2},{1,3},{2,0},{3,1},{4,6},{5,7},{6,4},{7,5},{8,10},{9,11},{10,... | collective-permute-start | bytes 196616 | tf_op jit(solution)/shard_map/ppermute | solution.py:31
  93.1 14.0 %collective-permute-start.35 = (f32[64,256]{1,0:T(8,128)S(1)}, f32[64,256]{1,0:T(8,128)S(1)}, u32[]{:S(2)}, u32[]{:S(2)}) collective-permute-start(f32[64,256]{1,0:T(8,128)S(1)} %fusion.7), channel_id=1, source_target_pairs={{0,3},{1,2},{2,1},{3,0},{4,7},{5,6},{6,5},{7,4},{8,11},{9,10},{10,... | collective-permute-start | bytes 196616 | tf_op jit(solution)/shard_map/ppermute | solution.py:31
  95.5 8.6 %collective-permute-start.33 = (f32[64,256]{1,0:T(8,128)S(1)}, f32[64,256]{1,0:T(8,128)S(1)}, u32[]{:S(2)}, u32[]{:S(2)}) collective-permute-start(f32[64,256]{1,0:T(8,128)S(1)} %fusion.7), channel_id=1, source_target_pairs={{0,1},{1,0},{2,3},{3,2},{4,5},{5,4},{6,7},{7,6},{8,9},{9,8},{10,11... | collective-permute-start | bytes 196616 | tf_op jit(solution)/shard_map/ppermute | solution.py:31
  98.7 8.7 %collective-permute-start.34 = (f32[64,256]{1,0:T(8,128)S(1)}, f32[64,256]{1,0:T(8,128)S(1)}, u32[]{:S(2)}, u32[]{:S(2)}) collective-permute-start(f32[64,256]{1,0:T(8,128)S(1)} %fusion.7), channel_id=1, source_target_pairs={{0,2},{1,3},{2,0},{3,1},{4,6},{5,7},{6,4},{7,5},{8,10},{9,11},{10,... | collective-permute-start | bytes 196616 | tf_op jit(solution)/shard_map/ppermute | solution.py:31
  102.0 10.9 %collective-permute-start.47 = (f32[64,256]{1,0:T(8,128)S(1)}, f32[64,256]{1,0:T(8,128)S(1)}, u32[]{:S(2)}, u32[]{:S(2)}) collective-permute-start(f32[64,256]{1,0:T(8,128)S(1)} %fusion.2), channel_id=1, source_target_pairs={{0,3},{1,2},{2,1},{3,0},{4,7},{5,6},{6,5},{7,4},{8,11},{9,10},{10,... | collective-permute-start | bytes 196616 | tf_op jit(solution)/shard_map/ppermute | solution.py:31
  104.1 6.1 %collective-permute-start.45 = (f32[64,256]{1,0:T(8,128)S(1)}, f32[64,256]{1,0:T(8,128)S(1)}, u32[]{:S(2)}, u32[]{:S(2)}) collective-permute-start(f32[64,256]{1,0:T(8,128)S(1)} %fusion.2), channel_id=1, source_target_pairs={{0,1},{1,0},{2,3},{3,2},{4,5},{5,4},{6,7},{7,6},{8,9},{9,8},{10,11... | collective-permute-start | bytes 196616 | tf_op jit(solution)/shard_map/ppermute | solution.py:31
  104.1 9.1 %collective-permute-start.46 = (f32[64,256]{1,0:T(8,128)S(1)}, f32[64,256]{1,0:T(8,128)S(1)}, u32[]{:S(2)}, u32[]{:S(2)}) collective-permute-start(f32[64,256]{1,0:T(8,128)S(1)} %fusion.2), channel_id=1, source_target_pairs={{0,2},{1,3},{2,0},{3,1},{4,6},{5,7},{6,4},{7,5},{8,10},{9,11},{10,... | collective-permute-start | bytes 196616 | tf_op jit(solution)/shard_map/ppermute | solution.py:31
  107.7 7.2 %collective-permute-start.44 = (f32[64,256]{1,0:T(8,128)S(1)}, f32[64,256]{1,0:T(8,128)S(1)}, u32[]{:S(2)}, u32[]{:S(2)}) collective-permute-start(f32[64,256]{1,0:T(8,128)S(1)} %fusion.5), channel_id=1, source_target_pairs={{0,3},{1,2},{2,1},{3,0},{4,7},{5,6},{6,5},{7,4},{8,11},{9,10},{10,... | collective-permute-start | bytes 196616 | tf_op jit(solution)/shard_map/ppermute | solution.py:31
  110.1 4.5 %collective-permute-start.42 = (f32[64,256]{1,0:T(8,128)S(1)}, f32[64,256]{1,0:T(8,128)S(1)}, u32[]{:S(2)}, u32[]{:S(2)}) collective-permute-start(f32[64,256]{1,0:T(8,128)S(1)} %fusion.5), channel_id=1, source_target_pairs={{0,1},{1,0},{2,3},{3,2},{4,5},{5,4},{6,7},{7,6},{8,9},{9,8},{10,11... | collective-permute-start | bytes 196616 | tf_op jit(solution)/shard_map/ppermute | solution.py:31
  110.2 5.2 %collective-permute-start.43 = (f32[64,256]{1,0:T(8,128)S(1)}, f32[64,256]{1,0:T(8,128)S(1)}, u32[]{:S(2)}, u32[]{:S(2)}) collective-permute-start(f32[64,256]{1,0:T(8,128)S(1)} %fusion.5), channel_id=1, source_target_pairs={{0,2},{1,3},{2,0},{3,1},{4,6},{5,7},{6,4},{7,5},{8,10},{9,11},{10,... | collective-permute-start | bytes 196616 | tf_op jit(solution)/shard_map/ppermute | solution.py:31
  115.9 1.4 collective-permute-start.48
  117.3 6.3 %collective-permute-start.51 = (f32[2,16,512]{2,1,0:T(8,128)S(1)}, f32[2,16,512]{2,1,0:T(8,128)S(1)}, u32[]{:S(2)}, u32[]{:S(2)}) collective-permute-start(f32[2,16,512]{2,1,0:T(8,128)S(1)} %get-tuple-element.25), channel_id=1, source_target_pairs={{0,24},{4,28},{8,16},{12,20},{16,8},{20,12},{24,0},{28,4},{1,25},{... | collective-permute-start | bytes 196616 | tf_op jit(solution)/shard_map/ppermute | solution.py:74
  120.9 4.3 %collective-permute-start.50 = (f32[2,16,512]{2,1,0:T(8,128)S(1)}, f32[2,16,512]{2,1,0:T(8,128)S(1)}, u32[]{:S(2)}, u32[]{:S(2)}) collective-permute-start(f32[2,16,512]{2,1,0:T(8,128)S(1)} %get-tuple-element.24), channel_id=1, source_target_pairs={{0,16},{4,20},{8,24},{12,28},{16,0},{20,4},{24,8},{28,12},{1,17},{... | collective-permute-start | bytes 196616 | tf_op jit(solution)/shard_map/ppermute | solution.py:74
  121.4 4.3 %collective-permute-start.49 = (f32[2,16,512]{2,1,0:T(8,128)S(1)}, f32[2,16,512]{2,1,0:T(8,128)S(1)}, u32[]{:S(2)}, u32[]{:S(2)}) collective-permute-start(f32[2,16,512]{2,1,0:T(8,128)S(1)} %get-tuple-element.23), channel_id=1, source_target_pairs={{0,8},{4,12},{8,0},{12,4},{16,24},{20,28},{24,16},{28,20},{1,9},{5... | collective-permute-start | bytes 196616 | tf_op jit(solution)/shard_map/ppermute | solution.py:74
  129.8 22.4 %copy-start.6 = (f32[1,256,128]{1,2,0:T(8,128)S(1)}, f32[1,256,128]{1,2,0:T(8,128)}, u32[]{:S(2)}) copy-start(f32[1,256,128]{1,2,0:T(8,128)} %maximum_bitcast_fusion.1) | copy-start | bytes 393220
  132.0 7.1 %collective-permute-start.54 = (f32[16,1280]{1,0:T(8,128)S(1)}, f32[16,1280]{1,0:T(8,128)S(1)}, u32[]{:S(2)}, u32[]{:S(2)}) collective-permute-start(f32[16,1280]{1,0:T(8,128)S(1)} %get-tuple-element.36), channel_id=1, source_target_pairs={{0,3},{1,2},{2,1},{3,0},{4,7},{5,6},{6,5},{7,4},{8,11},{9,10},{10,... | collective-permute-start | bytes 245768 | tf_op jit(solution)/shard_map/ppermute | solution.py:31
  133.3 8.3 %collective-permute-start.53 = (f32[16,1280]{1,0:T(8,128)S(1)}, f32[16,1280]{1,0:T(8,128)S(1)}, u32[]{:S(2)}, u32[]{:S(2)}) collective-permute-start(f32[16,1280]{1,0:T(8,128)S(1)} %get-tuple-element.35), channel_id=1, source_target_pairs={{0,2},{1,3},{2,0},{3,1},{4,6},{5,7},{6,4},{7,5},{8,10},{9,11},{10,... | collective-permute-start | bytes 245768 | tf_op jit(solution)/shard_map/ppermute | solution.py:31
  134.3 7.3 %collective-permute-start.52 = (f32[16,1280]{1,0:T(8,128)S(1)}, f32[16,1280]{1,0:T(8,128)S(1)}, u32[]{:S(2)}, u32[]{:S(2)}) collective-permute-start(f32[16,1280]{1,0:T(8,128)S(1)} %get-tuple-element.34), channel_id=1, source_target_pairs={{0,1},{1,0},{2,3},{3,2},{4,5},{5,4},{6,7},{7,6},{8,9},{9,8},{10,11... | collective-permute-start | bytes 245768 | tf_op jit(solution)/shard_map/ppermute | solution.py:31
  143.4 6.0 %collective-permute-start.57 = (f32[16,256]{1,0:T(8,128)S(1)}, f32[16,256]{1,0:T(8,128)S(1)}, u32[]{:S(2)}, u32[]{:S(2)}) collective-permute-start(f32[16,256]{1,0:T(8,128)S(1)} %fusion.26), channel_id=1, source_target_pairs={{0,3},{1,2},{2,1},{3,0},{4,7},{5,6},{6,5},{7,4},{8,11},{9,10},{10,... | collective-permute-start | bytes 49160 | tf_op jit(solution)/shard_map/ppermute | solution.py:31
  145.2 3.9 %collective-permute-start.55 = (f32[16,256]{1,0:T(8,128)S(1)}, f32[16,256]{1,0:T(8,128)S(1)}, u32[]{:S(2)}, u32[]{:S(2)}) collective-permute-start(f32[16,256]{1,0:T(8,128)S(1)} %fusion.26), channel_id=1, source_target_pairs={{0,1},{1,0},{2,3},{3,2},{4,5},{5,4},{6,7},{7,6},{8,9},{9,8},{10,11... | collective-permute-start | bytes 49160 | tf_op jit(solution)/shard_map/ppermute | solution.py:31
  145.2 4.6 %collective-permute-start.56 = (f32[16,256]{1,0:T(8,128)S(1)}, f32[16,256]{1,0:T(8,128)S(1)}, u32[]{:S(2)}, u32[]{:S(2)}) collective-permute-start(f32[16,256]{1,0:T(8,128)S(1)} %fusion.26), channel_id=1, source_target_pairs={{0,2},{1,3},{2,0},{3,1},{4,6},{5,7},{6,4},{7,5},{8,10},{9,11},{10,... | collective-permute-start | bytes 49160 | tf_op jit(solution)/shard_map/ppermute | solution.py:31
  150.1 7.4 %collective-permute-start.60 = (f32[16,256]{1,0:T(8,128)S(1)}, f32[16,256]{1,0:T(8,128)S(1)}, u32[]{:S(2)}, u32[]{:S(2)}) collective-permute-start(f32[16,256]{1,0:T(8,128)S(1)} %slice_subtract_fusion), channel_id=1, source_target_pairs={{0,3},{1,2},{2,1},{3,0},{4,7},{5,6},{6,5},{7,4},{8,11},{9,10},{10,... | collective-permute-start | bytes 49160 | tf_op jit(solution)/shard_map/ppermute | solution.py:31
  155.1 4.6 %collective-permute-start.59 = (f32[16,256]{1,0:T(8,128)S(1)}, f32[16,256]{1,0:T(8,128)S(1)}, u32[]{:S(2)}, u32[]{:S(2)}) collective-permute-start(f32[16,256]{1,0:T(8,128)S(1)} %slice_subtract_fusion), channel_id=1, source_target_pairs={{0,2},{1,3},{2,0},{3,1},{4,6},{5,7},{6,4},{7,5},{8,10},{9,11},{10,... | collective-permute-start | bytes 49160 | tf_op jit(solution)/shard_map/ppermute | solution.py:31
  156.5 4.4 %collective-permute-start.58 = (f32[16,256]{1,0:T(8,128)S(1)}, f32[16,256]{1,0:T(8,128)S(1)}, u32[]{:S(2)}, u32[]{:S(2)}) collective-permute-start(f32[16,256]{1,0:T(8,128)S(1)} %slice_subtract_fusion), channel_id=1, source_target_pairs={{0,1},{1,0},{2,3},{3,2},{4,5},{5,4},{6,7},{7,6},{8,9},{9,8},{10,11... | collective-permute-start | bytes 49160 | tf_op jit(solution)/shard_map/ppermute | solution.py:31
  (10 other events, 107.7 us)

commit v8 on v7

v8 whole, which is shorter than its diff:
```python
import jax
import jax.numpy as jnp
from jax import lax
from jax.experimental import pallas as pl
from jax.experimental.pallas import tpu as pltpu
from jax.sharding import PartitionSpec as P

high = lax.Precision.HIGH


def contract_last(left, right):
    return lax.dot_general(
        left,
        right,
        (((left.ndim - 1,), (right.ndim - 1,)), ((), ())),
        precision=high,
        preferred_element_type=jnp.float32,
    )


def partner(index, distance, count):
    if count & (count - 1):
        return lax.rem(index - distance + 2 * count, count)
    return index ^ abs(distance)


def send(value, axis, distance):
    count = lax.axis_size(axis)
    if count & (count - 1):
        pairs = [(i, (i + distance) % count) for i in range(count)]
    else:
        pairs = [(i, i ^ distance) for i in range(count)]
    return lax.ppermute(value, axis, pairs)


def gather_rows(value):
    members = lax.axis_size("grp")
    me = lax.axis_index("grp")
    rows = value.shape[1]
    pieces = [(me * rows, value)]
    for distance in range(1, members):
        owner = partner(me, distance, members)
        pieces.append((owner * rows, send(value, "grp", distance)))
    return pieces


def columns_of(factor, index, offset, width):
    lead = factor.ndim - 3
    begin = (0,) * lead + (index, 0, offset)
    size = (1,) * (lead + 1) + (factor.shape[-2], width)
    return lax.dynamic_slice(factor, begin, size).reshape(factor.shape[-2], width)


def apply_rows(factor, index, pieces):
    total = None
    for offset, piece in pieces:
        term = contract_last(piece, columns_of(factor, index, offset, piece.shape[1]))
        total = term if total is None else total + term
    return total


def assemble(pieces, order):
    whole = jnp.zeros((pieces[0][1].shape[0], order), jnp.float32)
    for offset, piece in pieces:
        whole = lax.dynamic_update_slice_in_dim(whole, piece, offset, 1)
    return whole


def swap(value, axis, distance, block):
    count = lax.axis_size(axis)
    outer = count // block
    if outer & (outer - 1):
        pairs = [(i, (i // block + distance) % outer * block + i % block) for i in range(count)]
    else:
        pairs = [(i, (i // block ^ distance) * block + i % block) for i in range(count)]
    return lax.ppermute(value, axis, pairs)


VMEM = pl.BlockSpec(memory_space=pltpu.VMEM)
SMEM = pl.BlockSpec(memory_space=pltpu.SMEM)


def local_kernel(body, outs, operands, specs=None, flops=0, scratch=()):
    size = sum(o.size * o.dtype.itemsize for o in list(outs) + list(operands))
    return pl.pallas_call(
        body,
        out_shape=list(outs),
        in_specs=specs or [VMEM] * len(operands),
        out_specs=[VMEM] * len(outs),
        scratch_shapes=list(scratch),
        cost_estimate=pl.CostEstimate(flops=flops, bytes_accessed=size, transcendentals=0),
    )(*operands)


def float_array(*shape):
    return jax.ShapeDtypeStruct(shape, jnp.float32)


def high_low(value):
    top = value.astype(jnp.bfloat16)
    return top, (value - top.astype(jnp.float32)).astype(jnp.bfloat16)


def split_product(left, top, rest):
    def dot(x, y):
        return lax.dot_general(
            x, y, (((1,), (1,)), ((), ())), preferred_element_type=jnp.float32
        )

    left_top, left_rest = high_low(left)
    return dot(left_top, top) + (dot(left_top, rest) + dot(left_rest, top))


def leaf_shape():
    groups = lax.axis_size("leaf")
    inner = 2 if groups % 2 == 0 else 1
    return groups // inner, inner


def pack_terms(early, late, sources, blocks, count, last, tile_rows):
    outer, inner = leaf_shape()
    slots = sources.shape[-1]
    depth = early[0].shape[0]
    streams = len(early)
    part = depth * streams // (outer * inner)
    width = (slots + 1) * tile_rows

    def body(*refs):
        early_refs, late_refs = refs[:streams], refs[streams : 2 * streams]
        source_ref, block_ref, count_ref = refs[2 * streams : 2 * streams + 3]
        outs = refs[2 * streams + 3 : -1]
        terms = refs[-1]
        lanes = lax.broadcasted_iota(jnp.int32, (depth, tile_rows), 1)
        tag = jnp.full((depth, tile_rows), -1.0, jnp.float32)
        for m in range(slots):
            value = jnp.where(m < count_ref[0, 0], block_ref[0, 0, m], -1).astype(jnp.float32)
            tag = jnp.where(lanes == m, value, tag)
        for i in range(streams):
            rows = slice(i * depth, (i + 1) * depth)
            for m in range(slots):
                at = slice(m * tile_rows, (m + 1) * tile_rows)
                terms[rows, at] = jnp.where(
                    source_ref[0, 0, m] == last, late_refs[i][:, at], early_refs[i][:, at]
                )
            terms[rows, slots * tile_rows :] = tag
        inside = lax.rem(lax.axis_index("leaf"), inner)
        for o in range(outer):
            cut = [
                terms[(o * inner + i) * part : (o * inner + i + 1) * part, :]
                for i in range(inner)
            ]
            for i in range(inner):
                outs[i][o] = jnp.where(inside == 0, cut[i], cut[inner - 1 - i])

    return local_kernel(
        body,
        [float_array(outer, part, width)] * inner,
        [*early, *late, sources, blocks, count],
        [VMEM] * (2 * streams) + [SMEM] * 3,
        scratch=[pltpu.VMEM((streams * depth, width), jnp.float32)],
    )


def leaf_exchange(packed):
    outer, inner = leaf_shape()
    part, width = packed[0].shape[1:]
    held = [packed[0]]
    if inner == 2:
        pairs = [(i, i ^ 1) for i in range(outer * inner)]
        held.append(lax.ppermute(packed[1], "leaf", pairs))

    def body(*refs):
        outside = lax.div(lax.axis_index("leaf"), inner)
        for distance in range(outer):
            target = partner(outside, -distance, outer) if distance else outside
            for i in range(inner):
                refs[inner + distance][i] = refs[i][target]

    portions = local_kernel(body, [float_array(inner, part, width)] * outer, held)
    return [portions[0]] + [
        swap(portions[distance], "leaf", distance, inner) for distance in range(1, outer)
    ]


def share_out(received, rhs_turned, order, slots, tile_rows):
    members = lax.axis_size("grp")
    ancestors, part, rows = rhs_turned.shape
    inner = received[0].shape[0]
    block_count = ancestors * order // tile_rows
    width = order + (ancestors - 1) * rows

    def body(*refs):
        sources = refs[: len(received)]
        rhs_ref = refs[len(received)]
        outs = refs[len(received) + 1 : -1]
        share = refs[-1]
        me = lax.axis_index("grp")
        totals = [jnp.zeros((part, tile_rows), jnp.float32) for _ in range(block_count)]
        for source in sources:
            for i in range(inner):
                for m in range(slots):
                    tile = source[i, :, m * tile_rows : (m + 1) * tile_rows]
                    tag = source[i, :, slots * tile_rows + m : slots * tile_rows + m + 1]
                    tag = jnp.broadcast_to(tag, tile.shape)
                    for q in range(block_count):
                        totals[q] = totals[q] + jnp.where(tag == float(q), tile, 0.0)
        for q in range(block_count):
            share[:, q * tile_rows : (q + 1) * tile_rows] = -totals[q]
        for a in range(ancestors):
            for j in range(members):
                at = slice(a * order + j * rows, a * order + (j + 1) * rows)
                share[:, at] = share[:, at] + jnp.where(me == j, rhs_ref[a], 0.0)
        for distance in range(members):
            target = partner(me, -distance, members) if distance else me
            out = outs[distance]
            out[:, :order] = share[:, :order]
            for a in range(1, ancestors):
                value = jnp.zeros((part, rows), jnp.float32)
                for j in range(members):
                    at = slice(a * order + j * rows, a * order + (j + 1) * rows)
                    value = jnp.where(target == j, share[:, at], value)
                out[:, order + (a - 1) * rows : order + a * rows] = value

    return local_kernel(
        body,
        [float_array(part, width)] * members,
        [*received, rhs_turned],
        scratch=[pltpu.VMEM((part, ancestors * order), jnp.float32)],
    )


def split_factors(factors, after):
    count = len(factors)

    def body(*refs):
        for i in range(count):
            top, rest = high_low(refs[i][...])
            refs[count + 1 + 2 * i][...] = top
            refs[count + 2 + 2 * i][...] = rest

    outs = []
    for factor in factors:
        outs += [jax.ShapeDtypeStruct(factor.shape, jnp.bfloat16)] * 2
    return local_kernel(
        body,
        outs,
        [*factors, after],
        [VMEM] * count + [pl.BlockSpec(memory_space=pl.ANY)],
        flops=4 * sum(f.size for f in factors),
    )


def solve_first(payloads, top, rest):
    part, width = payloads[0].shape
    rows, order = top.shape[1:]

    def body(*refs):
        sums = refs[: len(payloads)]
        top_ref, rest_ref, out, left = refs[len(payloads) :]
        total = sums[0][...]
        for ref in sums[1:]:
            total = total + ref[...]
        out[...] = split_product(total[:, :order], top_ref[0], rest_ref[0])
        left[...] = total[:, order:]

    return local_kernel(
        body,
        [float_array(part, rows), float_array(part, width - order)],
        [*payloads, top, rest],
        flops=6 * part * rows * order,
    )


def apply_split(pieces, top, rest, index, base=None, begin=0):
    members = lax.axis_size("grp")
    part, width = pieces[0].shape
    rows, order = top.shape[1:]
    extra = [] if base is None else [base]

    def body(*refs):
        held = refs[:members]
        top_ref, rest_ref = refs[members : members + 2]
        out, whole = refs[-2:]
        me = lax.axis_index("grp")
        for j in range(members):
            value = jnp.zeros((part, width), jnp.float32)
            for distance in range(members):
                owner = partner(me, distance, members) if distance else me
                value = jnp.where(owner == j, held[distance][...], value)
            whole[:, j * width : (j + 1) * width] = value
        result = split_product(whole[...], top_ref[index], rest_ref[index])
        if extra:
            result = refs[members + 2][:, begin : begin + rows] - result
        out[...] = result

    return local_kernel(
        body,
        [float_array(part, rows)],
        [*pieces, top, rest, *extra],
        flops=6 * part * rows * order,
        scratch=[pltpu.VMEM((part, order), jnp.float32)],
    )[0]


def on_device(
    rhs_local,
    diag_inv_local,
    sub_local,
    tiles,
    tile_block,
    tile_source,
    tile_count,
    rhs_anc,
    diag_inv_anc,
    sub_anc,
):
    rhs_group = rhs_local[0]
    supernodes = rhs_group.shape[0]
    order = diag_inv_local.shape[-1]
    rhs_count = rhs_group.shape[-1]
    members = lax.axis_size("grp")
    rows = order // members

    tiles_mine = tiles[0, 0]
    slots, tile_rows = tiles_mine.shape[:2]
    sources = tile_source[0, 0]

    streams = 2 if rhs_count % 16 == 0 else 1
    depth = rhs_count // streams
    first_rhs = jnp.transpose(lax.optimization_barrier(rhs_group[0]))
    first_factor = lax.optimization_barrier(diag_inv_local[0, 0])
    rhs_wide = jnp.swapaxes(rhs_group[1:], 1, 2)
    split = [rhs_wide[:, i * depth : (i + 1) * depth] for i in range(streams)]
    solved = []
    residuals = [first_rhs[i * depth : (i + 1) * depth] for i in range(streams)]
    chosen = [jnp.zeros((slots, depth, order), jnp.float32) for _ in range(streams)]
    for current in range(supernodes):
        factor, index = (diag_inv_local, current) if current else (first_factor[None], 0)
        owned = [apply_rows(factor, index, gather_rows(r)) for r in residuals]
        solved.append(jnp.transpose(jnp.concatenate(owned, axis=0)))
        held = [gather_rows(value) for value in owned]
        if current + 1 < supernodes:
            residuals = [
                portion[current] - apply_rows(sub_local, current, pieces)
                for portion, pieces in zip(split, held)
            ]
            chosen = [
                jnp.where((sources == current)[:, None, None], assemble(pieces, order)[None], old)
                for pieces, old in zip(held, chosen)
            ]

    flat_tiles = tiles_mine.reshape(slots * tile_rows, order)
    early = []
    late = []
    for pieces, picked in zip(held, chosen):
        early.append(
            jnp.concatenate(
                [contract_last(picked[m], tiles_mine[m]) for m in range(slots)], axis=1
            )
        )
        late.append(apply_rows(flat_tiles[None], 0, pieces))
    packed = pack_terms(
        early, late, tile_source, tile_block, tile_count, supernodes - 1, tile_rows
    )
    received = leaf_exchange(packed)
    shares = share_out(received, jnp.swapaxes(rhs_anc, 1, 2), order, slots, tile_rows)
    payloads = [shares[0]] + [send(shares[d], "grp", d) for d in range(1, members)]
    inverse_top, inverse_rest, below_top, below_rest = split_factors(
        [diag_inv_anc, sub_anc], shares[0]
    )
    solution, left = solve_first(payloads, inverse_top, inverse_rest)
    solutions = [solution]
    for ancestor in range(1, rhs_anc.shape[0]):
        pieces = [piece for _, piece in gather_rows(solutions[-1])]
        residual = apply_split(
            pieces, below_top, below_rest, ancestor - 1, left, (ancestor - 1) * rows
        )
        pieces = [piece for _, piece in gather_rows(residual)]
        solutions.append(apply_split(pieces, inverse_top, inverse_rest, ancestor))
    solutions = jnp.swapaxes(jnp.stack(solutions), 1, 2)
    return (jnp.stack(solved)[None], solutions)


def solution(mesh):
    return jax.shard_map(
        on_device,
        mesh=mesh,
        in_specs=(
            P("leaf", None, "grp", None),
            P("leaf", None, "grp", None),
            P("leaf", None, "grp", None),
            P("leaf", "grp", None, None, None),
            P("leaf", "grp", None),
            P("leaf", "grp", None),
            P("leaf", "grp"),
            P(None, "grp", "leaf"),
            P(None, "grp", None),
            P(None, "grp", None),
        ),
        out_specs=(P("leaf", None, "grp", None), P(None, "grp", "leaf")),
        check_vma=False,
    )
```

time: 165 us -> 180 us (1.091)
  Pallas kernels: 0 us -> 17.3 us
  waiting for transfers between devices: 15.4 us -> 21.3 us
  matrix products: 37 us -> 31.9 us
  local copies, waits for them, and re-layouts: 12.1 us -> 9.7 us
    pallas_call x0 -> x7, Pallas kernels: none -> 17.3 us  [local_kernel(): pl.pallas_call(body, out_shape=list(outs), in_specs=specs or [VMEM] * len...]
    dot_general x79 -> x70, matrix products: 36 us -> 31.9 us  [contract_last(): lax.dot_general(left, right, (((left.ndim - 1,), (right.ndim - 1,)), ((),...]
    ppermute x57, waiting for transfers between devices: 11.9 us -> 15.9 us  [send(): return lax.ppermute(value, axis, pairs)]
    reshape x2 -> x0, local copies, waits for them, and re-layouts: 2.01 us -> none  [the longest x1 1 us: on_device(): summed = jnp.einsum('gmq,grmt->rqt', onehot, received[:, :, :width].resha...]
    squeeze x2, local copies, waits for them, and re-layouts: 1.52 us -> 3.37 us  [the longest x1 2.3 us: on_device(): first_factor = lax.optimization_barrier(diag_inv_local[0, 0])]
    unnamed x28 -> x48, local copies, waits for them, and re-layouts: 4.85 us -> 4.22 us
  transfers between devices with their start and end apart: 61 -> 61, of which waited for: 15 -> 12; matrix products, arithmetic and copies ran while one was open for 25% -> 25% of each run, Pallas kernels for 0% -> 2%
where the time goes in v8:
time: 180 us; the launch traced here: 179 us
  starting transfers between devices  88.5 us (49%)
  matrix products  31.9 us (18%)
  waiting for transfers between devices  21.3 us (12%)
  Pallas kernels  17.3 us (10%)
  local copies, waits for them, and re-layouts  9.7 us (5%)
  other arithmetic  7.7 us (4%)
  between operations  2.41 us (1%)
    ppermute x57, starting transfers between devices, send(): return lax.ppermute(value, axis, pairs)  85 us
    dot_general x70, matrix products, contract_last(): lax.dot_general(left, right, (((left.ndim - 1,), (right.ndim - 1,)), ((),...  31.9 us
    pallas_call x7, Pallas kernels, local_kernel(): pl.pallas_call(body, out_shape=list(outs), in_specs=specs or [VMEM] * len...  17.3 us
    ppermute x57, waiting for transfers between devices, send(): return lax.ppermute(value, axis, pairs)  15.9 us
    ppermute x3, waiting for transfers between devices, swap(): return lax.ppermute(value, axis, pairs)  4.37 us
    unnamed x48, local copies, waits for them, and re-layouts  4.22 us
  transfers between devices with their start and end apart: 61, of which 12 were waited for; matrix products, arithmetic and copies ran while one was open for 25% of the time, Pallas kernels for 2%

profile of v8, /device:TPU:0, one launch (start us, length us, event | category | flops | bytes accessed | tf_op | source)
XLA Modules:
  0.0 178.8 jit_solution(11419819026623255556)
XLA Ops:
  2.5 4.0 %collective-permute-start.1 = (f32[64,256]{0,1:T(8,128)}, f32[64,256]{0,1:T(8,128)}, u32[]{:S(2)}, u32[]{:S(2)}) collective-permute-start(f32[64,256]{0,1:T(8,128)} %get-tuple-element.36), channel_id=1, source_target_pairs={{0,2},{1,3},{2,0},{3,1},{4,6},{5,7},{6,4},{7,5},{8,10},{9,11},{10,... | collective-permute-start | bytes 196616 | tf_op jit(solution)/shard_map/ppermute | solution.py:33
  6.5 1.6 collective-permute-start
  8.1 1.9 %collective-permute-start.4 = (f32[64,256]{0,1:T(8,128)}, f32[64,256]{0,1:T(8,128)}, u32[]{:S(2)}, u32[]{:S(2)}) collective-permute-start(f32[64,256]{0,1:T(8,128)} %get-tuple-element.37), channel_id=1, source_target_pairs={{0,2},{1,3},{2,0},{3,1},{4,6},{5,7},{6,4},{7,5},{8,10},{9,11},{10,... | collective-permute-start | bytes 196616 | tf_op jit(solution)/shard_map/ppermute | solution.py:33
  10.0 2.5 %collective-permute-start.3 = (f32[64,256]{0,1:T(8,128)}, f32[64,256]{0,1:T(8,128)}, u32[]{:S(2)}, u32[]{:S(2)}) collective-permute-start(f32[64,256]{0,1:T(8,128)} %get-tuple-element.37), channel_id=1, source_target_pairs={{0,1},{1,0},{2,3},{3,2},{4,5},{5,4},{6,7},{7,6},{8,9},{9,8},{10,11... | collective-permute-start | bytes 196616 | tf_op jit(solution)/shard_map/ppermute | solution.py:33
  12.5 2.3 %slice_bitcast_fusion = f32[256,1024]{1,0:T(8,128)} fusion(f32[1,4,256,1024]{3,2,1,0:T(8,128)} %param.11), kind=kLoop, calls=%fused_computation.54 | loop fusion | bytes 2097152 | tf_op jit(solution)/shard_map/squeeze | solution.py:331
  14.8 1.9 %fusion.188 = f32[256,64]{0,1:T(8,128)} fusion(f32[256,1024]{1,0:T(8,128)} %slice_bitcast_fusion, s32[]{:T(128)S(6)} %select_n.27, f32[128,256]{0,1:T(8,128)S(1)} %bitcast.318), kind=kOutput, calls=%fused_computation.230 | convolution fusion | flops 25165824 | bytes 458756 | tf_op jit(solution)/shard_map/dot_general | solution.py:12
  16.7 1.8 %fusion.190 = f32[256,64]{0,1:T(8,128)} fusion(f32[256,1024]{1,0:T(8,128)} %slice_bitcast_fusion, s32[]{:T(128)S(6)} %select_n.27, f32[128,256]{0,1:T(8,128)S(1)} %bitcast.319), kind=kOutput, calls=%fused_computation.232 | convolution fusion | flops 25165824 | bytes 458756 | tf_op jit(solution)/shard_map/dot_general | solution.py:12
  22.3 1.6 convolution_add_fusion.29
  23.9 4.4 %collective-permute-done.5 = f32[64,256]{0,1:T(8,128)S(1)} collective-permute-done((f32[64,256]{0,1:T(8,128)}, f32[64,256]{0,1:T(8,128)S(1)}, u32[]{:S(2)}, u32[]{:S(2)}) %collective-permute-start.5) | collective-permute-done | bytes 65568 | tf_op jit(solution)/shard_map/ppermute | solution.py:33
  28.3 1.2 fusion.180
  29.6 1.3 constant_dynamic-update-slice_fusion.3
  30.8 1.4 collective-permute-start.14
  32.2 3.0 %collective-permute-start.13 = (f32[64,256]{1,0:T(8,128)S(1)}, f32[64,256]{1,0:T(8,128)S(1)}, u32[]{:S(2)}, u32[]{:S(2)}) collective-permute-start(f32[64,256]{1,0:T(8,128)S(1)} %bitcast.327), channel_id=1, source_target_pairs={{0,2},{1,3},{2,0},{3,1},{4,6},{5,7},{6,4},{7,5},{8,10},{9,11},{10,... | collective-permute-start | bytes 196616 | tf_op jit(solution)/shard_map/ppermute | solution.py:33
  35.8 1.3 fusion.182
  37.0 1.3 convolution_add_fusion.31
  38.7 1.3 constant_dynamic-update-slice_fusion.15
  40.3 2.4 %collective-permute-start.8 = (f32[64,256]{1,0:T(8,128)S(1)}, f32[64,256]{1,0:T(8,128)S(1)}, u32[]{:S(2)}, u32[]{:S(2)}) collective-permute-start(f32[64,256]{1,0:T(8,128)S(1)} %bitcast.330), channel_id=1, source_target_pairs={{0,3},{1,2},{2,1},{3,0},{4,7},{5,6},{6,5},{7,4},{8,11},{9,10},{10,... | collective-permute-start | bytes 196616 | tf_op jit(solution)/shard_map/ppermute | solution.py:33
  43.3 1.4 collective-permute-start.6
  45.9 2.4 %collective-permute-start.17 = (f32[64,256]{1,0:T(8,128)S(1)}, f32[64,256]{1,0:T(8,128)S(1)}, u32[]{:S(2)}, u32[]{:S(2)}) collective-permute-start(f32[64,256]{1,0:T(8,128)S(1)} %fusion.16), channel_id=1, source_target_pairs={{0,3},{1,2},{2,1},{3,0},{4,7},{5,6},{6,5},{7,4},{8,11},{9,10},{10,... | collective-permute-start | bytes 196616 | tf_op jit(solution)/shard_map/ppermute | solution.py:33
  48.4 2.0 %collective-permute-start.15 = (f32[64,256]{1,0:T(8,128)S(1)}, f32[64,256]{1,0:T(8,128)S(1)}, u32[]{:S(2)}, u32[]{:S(2)}) collective-permute-start(f32[64,256]{1,0:T(8,128)S(1)} %fusion.16), channel_id=1, source_target_pairs={{0,1},{1,0},{2,3},{3,2},{4,5},{5,4},{6,7},{7,6},{8,9},{9,8},{10,11... | collective-permute-start | bytes 196616 | tf_op jit(solution)/shard_map/ppermute | solution.py:33
  51.6 2.7 %collective-permute-start.11 = (f32[64,256]{1,0:T(8,128)S(1)}, f32[64,256]{1,0:T(8,128)S(1)}, u32[]{:S(2)}, u32[]{:S(2)}) collective-permute-start(f32[64,256]{1,0:T(8,128)S(1)} %fusion.19), channel_id=1, source_target_pairs={{0,3},{1,2},{2,1},{3,0},{4,7},{5,6},{6,5},{7,4},{8,11},{9,10},{10,... | collective-permute-start | bytes 196616 | tf_op jit(solution)/shard_map/ppermute | solution.py:33
  54.4 1.8 collective-permute-start.9
  57.5 2.7 %collective-permute-start.26 = (f32[64,256]{1,0:T(8,128)S(1)}, f32[64,256]{1,0:T(8,128)S(1)}, u32[]{:S(2)}, u32[]{:S(2)}) collective-permute-start(f32[64,256]{1,0:T(8,128)S(1)} %get-tuple-element.46), channel_id=1, source_target_pairs={{0,3},{1,2},{2,1},{3,0},{4,7},{5,6},{6,5},{7,4},{8,11},{9,10},{10,... | collective-permute-start | bytes 196616 | tf_op jit(solution)/shard_map/ppermute | solution.py:33
  60.2 1.7 collective-permute-start.24
  63.1 2.7 %collective-permute-start.20 = (f32[64,256]{1,0:T(8,128)S(1)}, f32[64,256]{1,0:T(8,128)S(1)}, u32[]{:S(2)}, u32[]{:S(2)}) collective-permute-start(f32[64,256]{1,0:T(8,128)S(1)} %get-tuple-element.52), channel_id=1, source_target_pairs={{0,3},{1,2},{2,1},{3,0},{4,7},{5,6},{6,5},{7,4},{8,11},{9,10},{10,... | collective-permute-start | bytes 196616 | tf_op jit(solution)/shard_map/ppermute | solution.py:33
  65.9 1.7 collective-permute-start.18
  68.8 2.7 %collective-permute-start.29 = (f32[64,256]{1,0:T(8,128)S(1)}, f32[64,256]{1,0:T(8,128)S(1)}, u32[]{:S(2)}, u32[]{:S(2)}) collective-permute-start(f32[64,256]{1,0:T(8,128)S(1)} %fusion.10), channel_id=1, source_target_pairs={{0,3},{1,2},{2,1},{3,0},{4,7},{5,6},{6,5},{7,4},{8,11},{9,10},{10,... | collective-permute-start | bytes 196616 | tf_op jit(solution)/shard_map/ppermute | solution.py:33
  71.5 1.7 collective-permute-start.27
  74.4 2.7 %collective-permute-start.23 = (f32[64,256]{1,0:T(8,128)S(1)}, f32[64,256]{1,0:T(8,128)S(1)}, u32[]{:S(2)}, u32[]{:S(2)}) collective-permute-start(f32[64,256]{1,0:T(8,128)S(1)} %fusion.13), channel_id=1, source_target_pairs={{0,3},{1,2},{2,1},{3,0},{4,7},{5,6},{6,5},{7,4},{8,11},{9,10},{10,... | collective-permute-start | bytes 196616 | tf_op jit(solution)/shard_map/ppermute | solution.py:33
  77.3 1.8 %collective-permute-start.21 = (f32[64,256]{1,0:T(8,128)S(1)}, f32[64,256]{1,0:T(8,128)S(1)}, u32[]{:S(2)}, u32[]{:S(2)}) collective-permute-start(f32[64,256]{1,0:T(8,128)S(1)} %fusion.13), channel_id=1, source_target_pairs={{0,1},{1,0},{2,3},{3,2},{4,5},{5,4},{6,7},{7,6},{8,9},{9,8},{10,11... | collective-permute-start | bytes 196616 | tf_op jit(solution)/shard_map/ppermute | solution.py:33
  80.3 2.7 %collective-permute-start.38 = (f32[64,256]{1,0:T(8,128)S(1)}, f32[64,256]{1,0:T(8,128)S(1)}, u32[]{:S(2)}, u32[]{:S(2)}) collective-permute-start(f32[64,256]{1,0:T(8,128)S(1)} %get-tuple-element.48), channel_id=1, source_target_pairs={{0,3},{1,2},{2,1},{3,0},{4,7},{5,6},{6,5},{7,4},{8,11},{9,10},{10,... | collective-permute-start | bytes 196616 | tf_op jit(solution)/shard_map/ppermute | solution.py:33
  83.1 1.7 collective-permute-start.36
  86.0 2.7 %collective-permute-start.32 = (f32[64,256]{1,0:T(8,128)S(1)}, f32[64,256]{1,0:T(8,128)S(1)}, u32[]{:S(2)}, u32[]{:S(2)}) collective-permute-start(f32[64,256]{1,0:T(8,128)S(1)} %get-tuple-element.54), channel_id=1, source_target_pairs={{0,3},{1,2},{2,1},{3,0},{4,7},{5,6},{6,5},{7,4},{8,11},{9,10},{10,... | collective-permute-start | bytes 196616 | tf_op jit(solution)/shard_map/ppermute | solution.py:33
  88.8 1.7 collective-permute-start.30
  91.7 2.7 %collective-permute-start.41 = (f32[64,256]{1,0:T(8,128)S(1)}, f32[64,256]{1,0:T(8,128)S(1)}, u32[]{:S(2)}, u32[]{:S(2)}) collective-permute-start(f32[64,256]{1,0:T(8,128)S(1)} %fusion.4), channel_id=1, source_target_pairs={{0,3},{1,2},{2,1},{3,0},{4,7},{5,6},{6,5},{7,4},{8,11},{9,10},{10,... | collective-permute-start | bytes 196616 | tf_op jit(solution)/shard_map/ppermute | solution.py:33
  94.5 1.8 %collective-permute-start.39 = (f32[64,256]{1,0:T(8,128)S(1)}, f32[64,256]{1,0:T(8,128)S(1)}, u32[]{:S(2)}, u32[]{:S(2)}) collective-permute-start(f32[64,256]{1,0:T(8,128)S(1)} %fusion.4), channel_id=1, source_target_pairs={{0,1},{1,0},{2,3},{3,2},{4,5},{5,4},{6,7},{7,6},{8,9},{9,8},{10,11... | collective-permute-start | bytes 196616 | tf_op jit(solution)/shard_map/ppermute | solution.py:33
  100.5 2.7 %collective-permute-start.35 = (f32[64,256]{1,0:T(8,128)S(1)}, f32[64,256]{1,0:T(8,128)S(1)}, u32[]{:S(2)}, u32[]{:S(2)}) collective-permute-start(f32[64,256]{1,0:T(8,128)S(1)} %fusion.7), channel_id=1, source_target_pairs={{0,3},{1,2},{2,1},{3,0},{4,7},{5,6},{6,5},{7,4},{8,11},{9,10},{10,... | collective-permute-start | bytes 196616 | tf_op jit(solution)/shard_map/ppermute | solution.py:33
  104.0 1.7 collective-permute-start.33
  106.6 2.7 %collective-permute-start.47 = (f32[64,256]{1,0:T(8,128)S(1)}, f32[64,256]{1,0:T(8,128)S(1)}, u32[]{:S(2)}, u32[]{:S(2)}) collective-permute-start(f32[64,256]{1,0:T(8,128)S(1)} %fusion.2), channel_id=1, source_target_pairs={{0,3},{1,2},{2,1},{3,0},{4,7},{5,6},{6,5},{7,4},{8,11},{9,10},{10,... | collective-permute-start | bytes 196616 | tf_op jit(solution)/shard_map/ppermute | solution.py:33
  109.3 1.5 collective-permute-done.33
  112.0 2.7 %collective-permute-start.44 = (f32[64,256]{1,0:T(8,128)S(1)}, f32[64,256]{1,0:T(8,128)S(1)}, u32[]{:S(2)}, u32[]{:S(2)}) collective-permute-start(f32[64,256]{1,0:T(8,128)S(1)} %fusion.5), channel_id=1, source_target_pairs={{0,3},{1,2},{2,1},{3,0},{4,7},{5,6},{6,5},{7,4},{8,11},{9,10},{10,... | collective-permute-start | bytes 196616 | tf_op jit(solution)/shard_map/ppermute | solution.py:33
  115.8 3.8 %collective-permute-done.42 = f32[64,256]{1,0:T(8,128)S(1)} collective-permute-done((f32[64,256]{1,0:T(8,128)S(1)}, f32[64,256]{1,0:T(8,128)S(1)}, u32[]{:S(2)}, u32[]{:S(2)}) %collective-permute-start.42) | collective-permute-done | bytes 65568 | tf_op jit(solution)/shard_map/ppermute | solution.py:33
  120.9 4.5 %collective-permute-done.43 = f32[64,256]{1,0:T(8,128)S(1)} collective-permute-done((f32[64,256]{1,0:T(8,128)S(1)}, f32[64,256]{1,0:T(8,128)S(1)}, u32[]{:S(2)}, u32[]{:S(2)}) %collective-permute-start.43) | collective-permute-done | bytes 65568 | tf_op jit(solution)/shard_map/ppermute | solution.py:33
  128.0 1.8 shard_map.113
  131.5 1.7 shard_map.114
  133.2 1.5 collective-permute-start.49
  134.7 1.5 collective-permute-start.50
  137.7 1.5 collective-permute-done.50.refs_2_
  139.3 2.5 %collective-permute-done.51.refs_3_ = f32[2,16,512]{2,1,0:T(8,128)} collective-permute-done((f32[2,16,512]{2,1,0:T(8,128)}, f32[2,16,512]{2,1,0:T(8,128)}, u32[]{:S(2)}, u32[]{:S(2)}) %collective-permute-start.51) | collective-permute-done | bytes 65568 | tf_op jit(solution)/shard_map/ppermute | solution.py:76
  141.8 2.1 %shard_map.115 = (f32[16,1280]{1,0:T(8,128)}, f32[16,1280]{1,0:T(8,128)}, f32[16,1280]{1,0:T(8,128)}, f32[16,1280]{1,0:T(8,128)}) custom-call(f32[2,16,512]{2,1,0:T(8,128)} %get-tuple-element.20.refs_0_, f32[2,16,512]{2,1,0:T(8,128)} %copy-done.17, f32[2,16,512]{2,1,0:T(8,128)} %copy-done.18, f32[2,16,512]{2,1,0:T(8,128)} %collective-permute-done.51.refs_3_, ...), custom_call_target="tpu_custom_call" | custom-call | bytes 622592 | tf_op jit(solution)/shard_map/pallas_call | solution.py:85
  143.8 1.6 collective-permute-start.53
  145.4 2.8 %collective-permute-start.54 = (f32[16,1280]{1,0:T(8,128)}, f32[16,1280]{1,0:T(8,128)}, u32[]{:S(2)}, u32[]{:S(2)}) collective-permute-start(f32[16,1280]{1,0:T(8,128)} %get-tuple-element.27), channel_id=1, source_target_pairs={{0,3},{1,2},{2,1},{3,0},{4,7},{5,6},{6,5},{7,4},{8,11},{9,10},{10,... | collective-permute-start | bytes 245768 | tf_op jit(solution)/shard_map/ppermute | solution.py:33
  148.2 1.5 maximum_bitcast_fusion.3
  149.8 3.8 %shard_map.116 = (bf16[2,256,1024]{2,1,0:T(8,128)(2,1)}, bf16[2,256,1024]{2,1,0:T(8,128)(2,1)}, bf16[1,256,1024]{2,1,0:T(8,128)(2,1)}, bf16[1,256,1024]{2,1,0:T(8,128)(2,1)}) custom-call(f32[2,256,1024]{2,1,0:T(8,128)} %refs_0_.1, f32[1,256,1024]{2,1,0:T(8,128)} %refs_1_.1, f32[16,1280]{1,0:T(8,128)} %get-tuple-element.24.refs_2_.refs_0_), custom_call_target="tpu_custom_call" | custom-call | flops 3145728 | bytes 6373376 | tf_op jit(solution)/shard_map/pallas_call | solution.py:85
  153.6 2.8 %shard_map.117 = (f32[16,256]{1,0:T(8,128)}, f32[16,256]{1,0:T(8,128)}) custom-call(f32[16,1280]{1,0:T(8,128)} %get-tuple-element.24.refs_2_.refs_0_, f32[16,1280]{1,0:T(8,128)} %collective-permute-done.52.refs_1_, f32[16,1280]{1,0:T(8,128)} %collective-permute-done.53.refs_2_, f32[16,1280]{1,0:T(8,128)} %collective-permute-done.54.refs_3_, ...), custom_call_target="tpu_custom_call" | custom-call | flops 25165824 | bytes 2457600 | tf_op jit(solution)/shard_map/pallas_call | solution.py:85
  156.4 1.2 collective-permute-start.57
  158.0 2.8 %collective-permute-start.55 = (f32[16,256]{1,0:T(8,128)}, f32[16,256]{1,0:T(8,128)}, u32[]{:S(2)}, u32[]{:S(2)}) collective-permute-start(f32[16,256]{1,0:T(8,128)} %get-tuple-element.30.refs_0_), channel_id=1, source_target_pairs={{0,1},{1,0},{2,3},{3,2},{4,5},{5,4},{6,7},{7,6},{8,9},{9,8},{10,11... | collective-permute-start | bytes 49160 | tf_op jit(solution)/shard_map/ppermute | solution.py:33
  162.9 2.4 %shard_map.118.refs_0_ = f32[16,256]{1,0:T(8,128)} custom-call(f32[16,256]{1,0:T(8,128)} %get-tuple-element.30.refs_0_, f32[16,256]{1,0:T(8,128)} %collective-permute-done.55.refs_1_, f32[16,256]{1,0:T(8,128)} %collective-permute-done.56.refs_2_, f32[16,256]{1,0:T(8,128)} %collective-permute-done.57.refs_3_, ...), custom_call_target="tpu_custom_call" | custom-call | flops 25165824 | bytes 1146880 | tf_op jit(solution)/shard_map/pallas_call | solution.py:85
  165.2 2.3 %collective-permute-start.60 = (f32[16,256]{1,0:T(8,128)}, f32[16,256]{1,0:T(8,128)S(1)}, u32[]{:S(2)}, u32[]{:S(2)}) collective-permute-start(f32[16,256]{1,0:T(8,128)} %shard_map.118.refs_0_), channel_id=1, source_target_pairs={{0,3},{1,2},{2,1},{3,0},{4,7},{5,6},{6,5},{7,4},{8,11},{9,10},{10,... | collective-permute-start | bytes 49160 | tf_op jit(solution)/shard_map/ppermute | solution.py:33
  167.6 1.1 collective-permute-start.59
  169.6 1.8 %maximum_bitcast_fusion = f32[1,4,256,128]{2,3,1,0:T(8,128)} fusion(f32[1,256,128]{1,2,0:T(8,128)} %maximum_bitcast_fusion.4, f32[1,256,128]{1,2,0:T(8,128)} %maximum_bitcast_fusion.3, f32[1,256,128]{1,2,0:T(8,128)S(1)} %copy-done.15, f32[1,256,128]{1,2,0:T(8,128)S(1)} %copy-done.14), kind=kLoop, calls=%fused_computation.57 | loop fusion | flops 393216 | bytes 1048576 | tf_op jit(solution)/shard_map/broadcast_in_dim | solution.py:381
  171.5 2.0 %copy.13 = f32[1,4,256,128]{3,2,1,0:T(8,128)} copy(f32[1,4,256,128]{2,3,1,0:T(8,128)} %maximum_bitcast_fusion) | data formatting | bytes 1048576
  174.7 2.7 %shard_map.119 = f32[16,256]{1,0:T(8,128)} custom-call(f32[16,256]{1,0:T(8,128)} %shard_map.118.refs_0_, f32[16,256]{1,0:T(8,128)} %copy-done.21, f32[16,256]{1,0:T(8,128)} %copy-done.20, f32[16,256]{1,0:T(8,128)} %copy-done.19, bf16[2,256,1024]{2,1,0:T(8,128)(2,1)} %get-tuple-element.28.refs_4_, bf16[2,256,1024]{2,1,0:T(8,128)(2,1)} %get-tuple-element.29.refs_5_), custom_call_target="tpu_custom_call" | custom-call | flops 25165824 | bytes 2179072 | tf_op jit(solution)/shard_map/pallas_call | solution.py:85
  177.4 1.3 maximum_bitcast_fusion.5
  (220 shorter events, 36.7 us)
Async XLA Ops:
  0.6 37.7 %copy-start = (f32[1,3,256,1024]{3,2,1,0:T(8,128)S(1)}, f32[1,3,256,1024]{3,2,1,0:T(8,128)}, u32[]{:S(2)}) copy-start(f32[1,3,256,1024]{3,2,1,0:T(8,128)} %param.12) | copy-start | bytes 9437188
  2.5 36.2 %collective-permute-start.1 = (f32[64,256]{0,1:T(8,128)}, f32[64,256]{0,1:T(8,128)}, u32[]{:S(2)}, u32[]{:S(2)}) collective-permute-start(f32[64,256]{0,1:T(8,128)} %get-tuple-element.36), channel_id=1, source_target_pairs={{0,2},{1,3},{2,0},{3,1},{4,6},{5,7},{6,4},{7,5},{8,10},{9,11},{10,... | collective-permute-start | bytes 196616 | tf_op jit(solution)/shard_map/ppermute | solution.py:33
  6.5 30.5 %collective-permute-start = (f32[64,256]{0,1:T(8,128)}, f32[64,256]{0,1:T(8,128)}, u32[]{:S(2)}, u32[]{:S(2)}) collective-permute-start(f32[64,256]{0,1:T(8,128)} %get-tuple-element.36), channel_id=1, source_target_pairs={{0,1},{1,0},{2,3},{3,2},{4,5},{5,4},{6,7},{7,6},{8,9},{9,8},{10,11... | collective-permute-start | bytes 196616 | tf_op jit(solution)/shard_map/ppermute | solution.py:33
  8.1 27.2 %collective-permute-start.2 = (f32[64,256]{0,1:T(8,128)}, f32[64,256]{0,1:T(8,128)}, u32[]{:S(2)}, u32[]{:S(2)}) collective-permute-start(f32[64,256]{0,1:T(8,128)} %get-tuple-element.36), channel_id=1, source_target_pairs={{0,3},{1,2},{2,1},{3,0},{4,7},{5,6},{6,5},{7,4},{8,11},{9,10},{10,... | collective-permute-start | bytes 196616 | tf_op jit(solution)/shard_map/ppermute | solution.py:33
  8.1 21.4 %collective-permute-start.4 = (f32[64,256]{0,1:T(8,128)}, f32[64,256]{0,1:T(8,128)}, u32[]{:S(2)}, u32[]{:S(2)}) collective-permute-start(f32[64,256]{0,1:T(8,128)} %get-tuple-element.37), channel_id=1, source_target_pairs={{0,2},{1,3},{2,0},{3,1},{4,6},{5,7},{6,4},{7,5},{8,10},{9,11},{10,... | collective-permute-start | bytes 196616 | tf_op jit(solution)/shard_map/ppermute | solution.py:33
  10.0 11.2 %collective-permute-start.3 = (f32[64,256]{0,1:T(8,128)}, f32[64,256]{0,1:T(8,128)}, u32[]{:S(2)}, u32[]{:S(2)}) collective-permute-start(f32[64,256]{0,1:T(8,128)} %get-tuple-element.37), channel_id=1, source_target_pairs={{0,1},{1,0},{2,3},{3,2},{4,5},{5,4},{6,7},{7,6},{8,9},{9,8},{10,11... | collective-permute-start | bytes 196616 | tf_op jit(solution)/shard_map/ppermute | solution.py:33
  21.2 7.1 %collective-permute-start.5 = (f32[64,256]{0,1:T(8,128)}, f32[64,256]{0,1:T(8,128)S(1)}, u32[]{:S(2)}, u32[]{:S(2)}) collective-permute-start(f32[64,256]{0,1:T(8,128)} %get-tuple-element.37), channel_id=1, source_target_pairs={{0,3},{1,2},{2,1},{3,0},{4,7},{5,6},{6,5},{7,4},{8,11},{9,10},{10,... | collective-permute-start | bytes 196616 | tf_op jit(solution)/shard_map/ppermute | solution.py:33
  30.8 14.2 %collective-permute-start.14 = (f32[64,256]{1,0:T(8,128)S(1)}, f32[64,256]{1,0:T(8,128)S(1)}, u32[]{:S(2)}, u32[]{:S(2)}) collective-permute-start(f32[64,256]{1,0:T(8,128)S(1)} %bitcast.326), channel_id=1, source_target_pairs={{0,3},{1,2},{2,1},{3,0},{4,7},{5,6},{6,5},{7,4},{8,11},{9,10},{10,... | collective-permute-start | bytes 196616 | tf_op jit(solution)/shard_map/ppermute | solution.py:33
  32.2 13.1 %collective-permute-start.13 = (f32[64,256]{1,0:T(8,128)S(1)}, f32[64,256]{1,0:T(8,128)S(1)}, u32[]{:S(2)}, u32[]{:S(2)}) collective-permute-start(f32[64,256]{1,0:T(8,128)S(1)} %bitcast.327), channel_id=1, source_target_pairs={{0,2},{1,3},{2,0},{3,1},{4,6},{5,7},{6,4},{7,5},{8,10},{9,11},{10,... | collective-permute-start | bytes 196616 | tf_op jit(solution)/shard_map/ppermute | solution.py:33
  35.3 8.0 %collective-permute-start.12 = (f32[64,256]{1,0:T(8,128)S(1)}, f32[64,256]{1,0:T(8,128)S(1)}, u32[]{:S(2)}, u32[]{:S(2)}) collective-permute-start(f32[64,256]{1,0:T(8,128)S(1)} %bitcast.328), channel_id=1, source_target_pairs={{0,1},{1,0},{2,3},{3,2},{4,5},{5,4},{6,7},{7,6},{8,9},{9,8},{10,11... | collective-permute-start | bytes 196616 | tf_op jit(solution)/shard_map/ppermute | solution.py:33
  40.3 10.4 %collective-permute-start.8 = (f32[64,256]{1,0:T(8,128)S(1)}, f32[64,256]{1,0:T(8,128)S(1)}, u32[]{:S(2)}, u32[]{:S(2)}) collective-permute-start(f32[64,256]{1,0:T(8,128)S(1)} %bitcast.330), channel_id=1, source_target_pairs={{0,3},{1,2},{2,1},{3,0},{4,7},{5,6},{6,5},{7,4},{8,11},{9,10},{10,... | collective-permute-start | bytes 196616 | tf_op jit(solution)/shard_map/ppermute | solution.py:33
  42.7 8.3 %collective-permute-start.7 = (f32[64,256]{1,0:T(8,128)S(1)}, f32[64,256]{1,0:T(8,128)S(1)}, u32[]{:S(2)}, u32[]{:S(2)}) collective-permute-start(f32[64,256]{1,0:T(8,128)S(1)} %bitcast.331), channel_id=1, source_target_pairs={{0,2},{1,3},{2,0},{3,1},{4,6},{5,7},{6,4},{7,5},{8,10},{9,11},{10,... | collective-permute-start | bytes 196616 | tf_op jit(solution)/shard_map/ppermute | solution.py:33
  43.3 5.1 %collective-permute-start.6 = (f32[64,256]{1,0:T(8,128)S(1)}, f32[64,256]{1,0:T(8,128)S(1)}, u32[]{:S(2)}, u32[]{:S(2)}) collective-permute-start(f32[64,256]{1,0:T(8,128)S(1)} %bitcast.332), channel_id=1, source_target_pairs={{0,1},{1,0},{2,3},{3,2},{4,5},{5,4},{6,7},{7,6},{8,9},{9,8},{10,11... | collective-permute-start | bytes 196616 | tf_op jit(solution)/shard_map/ppermute | solution.py:33
  45.9 10.6 %collective-permute-start.17 = (f32[64,256]{1,0:T(8,128)S(1)}, f32[64,256]{1,0:T(8,128)S(1)}, u32[]{:S(2)}, u32[]{:S(2)}) collective-permute-start(f32[64,256]{1,0:T(8,128)S(1)} %fusion.16), channel_id=1, source_target_pairs={{0,3},{1,2},{2,1},{3,0},{4,7},{5,6},{6,5},{7,4},{8,11},{9,10},{10,... | collective-permute-start | bytes 196616 | tf_op jit(solution)/shard_map/ppermute | solution.py:33
  48.4 8.5 %collective-permute-start.16 = (f32[64,256]{1,0:T(8,128)S(1)}, f32[64,256]{1,0:T(8,128)S(1)}, u32[]{:S(2)}, u32[]{:S(2)}) collective-permute-start(f32[64,256]{1,0:T(8,128)S(1)} %fusion.16), channel_id=1, source_target_pairs={{0,2},{1,3},{2,0},{3,1},{4,6},{5,7},{6,4},{7,5},{8,10},{9,11},{10,... | collective-permute-start | bytes 196616 | tf_op jit(solution)/shard_map/ppermute | solution.py:33
  48.4 6.0 %collective-permute-start.15 = (f32[64,256]{1,0:T(8,128)S(1)}, f32[64,256]{1,0:T(8,128)S(1)}, u32[]{:S(2)}, u32[]{:S(2)}) collective-permute-start(f32[64,256]{1,0:T(8,128)S(1)} %fusion.16), channel_id=1, source_target_pairs={{0,1},{1,0},{2,3},{3,2},{4,5},{5,4},{6,7},{7,6},{8,9},{9,8},{10,11... | collective-permute-start | bytes 196616 | tf_op jit(solution)/shard_map/ppermute | solution.py:33
  51.6 10.6 %collective-permute-start.11 = (f32[64,256]{1,0:T(8,128)S(1)}, f32[64,256]{1,0:T(8,128)S(1)}, u32[]{:S(2)}, u32[]{:S(2)}) collective-permute-start(f32[64,256]{1,0:T(8,128)S(1)} %fusion.19), channel_id=1, source_target_pairs={{0,3},{1,2},{2,1},{3,0},{4,7},{5,6},{6,5},{7,4},{8,11},{9,10},{10,... | collective-permute-start | bytes 196616 | tf_op jit(solution)/shard_map/ppermute | solution.py:33
  54.3 8.2 %collective-permute-start.10 = (f32[64,256]{1,0:T(8,128)S(1)}, f32[64,256]{1,0:T(8,128)S(1)}, u32[]{:S(2)}, u32[]{:S(2)}) collective-permute-start(f32[64,256]{1,0:T(8,128)S(1)} %fusion.19), channel_id=1, source_target_pairs={{0,2},{1,3},{2,0},{3,1},{4,6},{5,7},{6,4},{7,5},{8,10},{9,11},{10,... | collective-permute-start | bytes 196616 | tf_op jit(solution)/shard_map/ppermute | solution.py:33
  54.4 5.8 %collective-permute-start.9 = (f32[64,256]{1,0:T(8,128)S(1)}, f32[64,256]{1,0:T(8,128)S(1)}, u32[]{:S(2)}, u32[]{:S(2)}) collective-permute-start(f32[64,256]{1,0:T(8,128)S(1)} %fusion.19), channel_id=1, source_target_pairs={{0,1},{1,0},{2,3},{3,2},{4,5},{5,4},{6,7},{7,6},{8,9},{9,8},{10,11... | collective-permute-start | bytes 196616 | tf_op jit(solution)/shard_map/ppermute | solution.py:33
  57.5 10.4 %collective-permute-start.26 = (f32[64,256]{1,0:T(8,128)S(1)}, f32[64,256]{1,0:T(8,128)S(1)}, u32[]{:S(2)}, u32[]{:S(2)}) collective-permute-start(f32[64,256]{1,0:T(8,128)S(1)} %get-tuple-element.46), channel_id=1, source_target_pairs={{0,3},{1,2},{2,1},{3,0},{4,7},{5,6},{6,5},{7,4},{8,11},{9,10},{10,... | collective-permute-start | bytes 196616 | tf_op jit(solution)/shard_map/ppermute | solution.py:33
  60.2 8.0 %collective-permute-start.25 = (f32[64,256]{1,0:T(8,128)S(1)}, f32[64,256]{1,0:T(8,128)S(1)}, u32[]{:S(2)}, u32[]{:S(2)}) collective-permute-start(f32[64,256]{1,0:T(8,128)S(1)} %get-tuple-element.46), channel_id=1, source_target_pairs={{0,2},{1,3},{2,0},{3,1},{4,6},{5,7},{6,4},{7,5},{8,10},{9,11},{10,... | collective-permute-start | bytes 196616 | tf_op jit(solution)/shard_map/ppermute | solution.py:33
  60.2 5.7 %collective-permute-start.24 = (f32[64,256]{1,0:T(8,128)S(1)}, f32[64,256]{1,0:T(8,128)S(1)}, u32[]{:S(2)}, u32[]{:S(2)}) collective-permute-start(f32[64,256]{1,0:T(8,128)S(1)} %get-tuple-element.46), channel_id=1, source_target_pairs={{0,1},{1,0},{2,3},{3,2},{4,5},{5,4},{6,7},{7,6},{8,9},{9,8},{10,11... | collective-permute-start | bytes 196616 | tf_op jit(solution)/shard_map/ppermute | solution.py:33
  63.1 10.4 %collective-permute-start.20 = (f32[64,256]{1,0:T(8,128)S(1)}, f32[64,256]{1,0:T(8,128)S(1)}, u32[]{:S(2)}, u32[]{:S(2)}) collective-permute-start(f32[64,256]{1,0:T(8,128)S(1)} %get-tuple-element.52), channel_id=1, source_target_pairs={{0,3},{1,2},{2,1},{3,0},{4,7},{5,6},{6,5},{7,4},{8,11},{9,10},{10,... | collective-permute-start | bytes 196616 | tf_op jit(solution)/shard_map/ppermute | solution.py:33
  65.9 8.0 %collective-permute-start.19 = (f32[64,256]{1,0:T(8,128)S(1)}, f32[64,256]{1,0:T(8,128)S(1)}, u32[]{:S(2)}, u32[]{:S(2)}) collective-permute-start(f32[64,256]{1,0:T(8,128)S(1)} %get-tuple-element.52), channel_id=1, source_target_pairs={{0,2},{1,3},{2,0},{3,1},{4,6},{5,7},{6,4},{7,5},{8,10},{9,11},{10,... | collective-permute-start | bytes 196616 | tf_op jit(solution)/shard_map/ppermute | solution.py:33
  65.9 5.7 %collective-permute-start.18 = (f32[64,256]{1,0:T(8,128)S(1)}, f32[64,256]{1,0:T(8,128)S(1)}, u32[]{:S(2)}, u32[]{:S(2)}) collective-permute-start(f32[64,256]{1,0:T(8,128)S(1)} %get-tuple-element.52), channel_id=1, source_target_pairs={{0,1},{1,0},{2,3},{3,2},{4,5},{5,4},{6,7},{7,6},{8,9},{9,8},{10,11... | collective-permute-start | bytes 196616 | tf_op jit(solution)/shard_map/ppermute | solution.py:33
  68.8 10.6 %collective-permute-start.29 = (f32[64,256]{1,0:T(8,128)S(1)}, f32[64,256]{1,0:T(8,128)S(1)}, u32[]{:S(2)}, u32[]{:S(2)}) collective-permute-start(f32[64,256]{1,0:T(8,128)S(1)} %fusion.10), channel_id=1, source_target_pairs={{0,3},{1,2},{2,1},{3,0},{4,7},{5,6},{6,5},{7,4},{8,11},{9,10},{10,... | collective-permute-start | bytes 196616 | tf_op jit(solution)/shard_map/ppermute | solution.py:33
  71.5 8.2 %collective-permute-start.28 = (f32[64,256]{1,0:T(8,128)S(1)}, f32[64,256]{1,0:T(8,128)S(1)}, u32[]{:S(2)}, u32[]{:S(2)}) collective-permute-start(f32[64,256]{1,0:T(8,128)S(1)} %fusion.10), channel_id=1, source_target_pairs={{0,2},{1,3},{2,0},{3,1},{4,6},{5,7},{6,4},{7,5},{8,10},{9,11},{10,... | collective-permute-start | bytes 196616 | tf_op jit(solution)/shard_map/ppermute | solution.py:33
  71.5 5.8 %collective-permute-start.27 = (f32[64,256]{1,0:T(8,128)S(1)}, f32[64,256]{1,0:T(8,128)S(1)}, u32[]{:S(2)}, u32[]{:S(2)}) collective-permute-start(f32[64,256]{1,0:T(8,128)S(1)} %fusion.10), channel_id=1, source_target_pairs={{0,1},{1,0},{2,3},{3,2},{4,5},{5,4},{6,7},{7,6},{8,9},{9,8},{10,11... | collective-permute-start | bytes 196616 | tf_op jit(solution)/shard_map/ppermute | solution.py:33
  74.4 10.6 %collective-permute-start.23 = (f32[64,256]{1,0:T(8,128)S(1)}, f32[64,256]{1,0:T(8,128)S(1)}, u32[]{:S(2)}, u32[]{:S(2)}) collective-permute-start(f32[64,256]{1,0:T(8,128)S(1)} %fusion.13), channel_id=1, source_target_pairs={{0,3},{1,2},{2,1},{3,0},{4,7},{5,6},{6,5},{7,4},{8,11},{9,10},{10,... | collective-permute-start | bytes 196616 | tf_op jit(solution)/shard_map/ppermute | solution.py:33
  77.2 8.2 %collective-permute-start.22 = (f32[64,256]{1,0:T(8,128)S(1)}, f32[64,256]{1,0:T(8,128)S(1)}, u32[]{:S(2)}, u32[]{:S(2)}) collective-permute-start(f32[64,256]{1,0:T(8,128)S(1)} %fusion.13), channel_id=1, source_target_pairs={{0,2},{1,3},{2,0},{3,1},{4,6},{5,7},{6,4},{7,5},{8,10},{9,11},{10,... | collective-permute-start | bytes 196616 | tf_op jit(solution)/shard_map/ppermute | solution.py:33
  77.3 5.8 %collective-permute-start.21 = (f32[64,256]{1,0:T(8,128)S(1)}, f32[64,256]{1,0:T(8,128)S(1)}, u32[]{:S(2)}, u32[]{:S(2)}) collective-permute-start(f32[64,256]{1,0:T(8,128)S(1)} %fusion.13), channel_id=1, source_target_pairs={{0,1},{1,0},{2,3},{3,2},{4,5},{5,4},{6,7},{7,6},{8,9},{9,8},{10,11... | collective-permute-start | bytes 196616 | tf_op jit(solution)/shard_map/ppermute | solution.py:33
  80.3 10.4 %collective-permute-start.38 = (f32[64,256]{1,0:T(8,128)S(1)}, f32[64,256]{1,0:T(8,128)S(1)}, u32[]{:S(2)}, u32[]{:S(2)}) collective-permute-start(f32[64,256]{1,0:T(8,128)S(1)} %get-tuple-element.48), channel_id=1, source_target_pairs={{0,3},{1,2},{2,1},{3,0},{4,7},{5,6},{6,5},{7,4},{8,11},{9,10},{10,... | collective-permute-start | bytes 196616 | tf_op jit(solution)/shard_map/ppermute | solution.py:33
  83.1 8.0 %collective-permute-start.37 = (f32[64,256]{1,0:T(8,128)S(1)}, f32[64,256]{1,0:T(8,128)S(1)}, u32[]{:S(2)}, u32[]{:S(2)}) collective-permute-start(f32[64,256]{1,0:T(8,128)S(1)} %get-tuple-element.48), channel_id=1, source_target_pairs={{0,2},{1,3},{2,0},{3,1},{4,6},{5,7},{6,4},{7,5},{8,10},{9,11},{10,... | collective-permute-start | bytes 196616 | tf_op jit(solution)/shard_map/ppermute | solution.py:33
  83.1 5.7 %collective-permute-start.36 = (f32[64,256]{1,0:T(8,128)S(1)}, f32[64,256]{1,0:T(8,128)S(1)}, u32[]{:S(2)}, u32[]{:S(2)}) collective-permute-start(f32[64,256]{1,0:T(8,128)S(1)} %get-tuple-element.48), channel_id=1, source_target_pairs={{0,1},{1,0},{2,3},{3,2},{4,5},{5,4},{6,7},{7,6},{8,9},{9,8},{10,11... | collective-permute-start | bytes 196616 | tf_op jit(solution)/shard_map/ppermute | solution.py:33
  86.0 10.3 %collective-permute-start.32 = (f32[64,256]{1,0:T(8,128)S(1)}, f32[64,256]{1,0:T(8,128)S(1)}, u32[]{:S(2)}, u32[]{:S(2)}) collective-permute-start(f32[64,256]{1,0:T(8,128)S(1)} %get-tuple-element.54), channel_id=1, source_target_pairs={{0,3},{1,2},{2,1},{3,0},{4,7},{5,6},{6,5},{7,4},{8,11},{9,10},{10,... | collective-permute-start | bytes 196616 | tf_op jit(solution)/shard_map/ppermute | solution.py:33
  88.8 7.5 %collective-permute-start.31 = (f32[64,256]{1,0:T(8,128)S(1)}, f32[64,256]{1,0:T(8,128)S(1)}, u32[]{:S(2)}, u32[]{:S(2)}) collective-permute-start(f32[64,256]{1,0:T(8,128)S(1)} %get-tuple-element.54), channel_id=1, source_target_pairs={{0,2},{1,3},{2,0},{3,1},{4,6},{5,7},{6,4},{7,5},{8,10},{9,11},{10,... | collective-permute-start | bytes 196616 | tf_op jit(solution)/shard_map/ppermute | solution.py:33
  88.8 5.7 %collective-permute-start.30 = (f32[64,256]{1,0:T(8,128)S(1)}, f32[64,256]{1,0:T(8,128)S(1)}, u32[]{:S(2)}, u32[]{:S(2)}) collective-permute-start(f32[64,256]{1,0:T(8,128)S(1)} %get-tuple-element.54), channel_id=1, source_target_pairs={{0,1},{1,0},{2,3},{3,2},{4,5},{5,4},{6,7},{7,6},{8,9},{9,8},{10,11... | collective-permute-start | bytes 196616 | tf_op jit(solution)/shard_map/ppermute | solution.py:33
  91.7 14.3 %collective-permute-start.41 = (f32[64,256]{1,0:T(8,128)S(1)}, f32[64,256]{1,0:T(8,128)S(1)}, u32[]{:S(2)}, u32[]{:S(2)}) collective-permute-start(f32[64,256]{1,0:T(8,128)S(1)} %fusion.4), channel_id=1, source_target_pairs={{0,3},{1,2},{2,1},{3,0},{4,7},{5,6},{6,5},{7,4},{8,11},{9,10},{10,... | collective-permute-start | bytes 196616 | tf_op jit(solution)/shard_map/ppermute | solution.py:33
  94.4 11.9 %collective-permute-start.40 = (f32[64,256]{1,0:T(8,128)S(1)}, f32[64,256]{1,0:T(8,128)S(1)}, u32[]{:S(2)}, u32[]{:S(2)}) collective-permute-start(f32[64,256]{1,0:T(8,128)S(1)} %fusion.4), channel_id=1, source_target_pairs={{0,2},{1,3},{2,0},{3,1},{4,6},{5,7},{6,4},{7,5},{8,10},{9,11},{10,... | collective-permute-start | bytes 196616 | tf_op jit(solution)/shard_map/ppermute | solution.py:33
  94.5 9.5 %collective-permute-start.39 = (f32[64,256]{1,0:T(8,128)S(1)}, f32[64,256]{1,0:T(8,128)S(1)}, u32[]{:S(2)}, u32[]{:S(2)}) collective-permute-start(f32[64,256]{1,0:T(8,128)S(1)} %fusion.4), channel_id=1, source_target_pairs={{0,1},{1,0},{2,3},{3,2},{4,5},{5,4},{6,7},{7,6},{8,9},{9,8},{10,11... | collective-permute-start | bytes 196616 | tf_op jit(solution)/shard_map/ppermute | solution.py:33
  100.5 10.8 %collective-permute-start.35 = (f32[64,256]{1,0:T(8,128)S(1)}, f32[64,256]{1,0:T(8,128)S(1)}, u32[]{:S(2)}, u32[]{:S(2)}) collective-permute-start(f32[64,256]{1,0:T(8,128)S(1)} %fusion.7), channel_id=1, source_target_pairs={{0,3},{1,2},{2,1},{3,0},{4,7},{5,6},{6,5},{7,4},{8,11},{9,10},{10,... | collective-permute-start | bytes 196616 | tf_op jit(solution)/shard_map/ppermute | solution.py:33
  103.3 8.4 %collective-permute-start.34 = (f32[64,256]{1,0:T(8,128)S(1)}, f32[64,256]{1,0:T(8,128)S(1)}, u32[]{:S(2)}, u32[]{:S(2)}) collective-permute-start(f32[64,256]{1,0:T(8,128)S(1)} %fusion.7), channel_id=1, source_target_pairs={{0,2},{1,3},{2,0},{3,1},{4,6},{5,7},{6,4},{7,5},{8,10},{9,11},{10,... | collective-permute-start | bytes 196616 | tf_op jit(solution)/shard_map/ppermute | solution.py:33
  104.0 6.9 %collective-permute-start.33 = (f32[64,256]{1,0:T(8,128)S(1)}, f32[64,256]{1,0:T(8,128)S(1)}, u32[]{:S(2)}, u32[]{:S(2)}) collective-permute-start(f32[64,256]{1,0:T(8,128)S(1)} %fusion.7), channel_id=1, source_target_pairs={{0,1},{1,0},{2,3},{3,2},{4,5},{5,4},{6,7},{7,6},{8,9},{9,8},{10,11... | collective-permute-start | bytes 196616 | tf_op jit(solution)/shard_map/ppermute | solution.py:33
  106.6 20.2 %collective-permute-start.47 = (f32[64,256]{1,0:T(8,128)S(1)}, f32[64,256]{1,0:T(8,128)S(1)}, u32[]{:S(2)}, u32[]{:S(2)}) collective-permute-start(f32[64,256]{1,0:T(8,128)S(1)} %fusion.2), channel_id=1, source_target_pairs={{0,3},{1,2},{2,1},{3,0},{4,7},{5,6},{6,5},{7,4},{8,11},{9,10},{10,... | collective-permute-start | bytes 196616 | tf_op jit(solution)/shard_map/ppermute | solution.py:33
  109.3 17.8 %collective-permute-start.46 = (f32[64,256]{1,0:T(8,128)S(1)}, f32[64,256]{1,0:T(8,128)S(1)}, u32[]{:S(2)}, u32[]{:S(2)}) collective-permute-start(f32[64,256]{1,0:T(8,128)S(1)} %fusion.2), channel_id=1, source_target_pairs={{0,2},{1,3},{2,0},{3,1},{4,6},{5,7},{6,4},{7,5},{8,10},{9,11},{10,... | collective-permute-start | bytes 196616 | tf_op jit(solution)/shard_map/ppermute | solution.py:33
  110.8 15.6 %collective-permute-start.45 = (f32[64,256]{1,0:T(8,128)S(1)}, f32[64,256]{1,0:T(8,128)S(1)}, u32[]{:S(2)}, u32[]{:S(2)}) collective-permute-start(f32[64,256]{1,0:T(8,128)S(1)} %fusion.2), channel_id=1, source_target_pairs={{0,1},{1,0},{2,3},{3,2},{4,5},{5,4},{6,7},{7,6},{8,9},{9,8},{10,11... | collective-permute-start | bytes 196616 | tf_op jit(solution)/shard_map/ppermute | solution.py:33
  111.6 25.1 %copy-start.9 = (f32[64,256]{1,0:T(8,128)S(1)}, f32[64,256]{1,0:T(8,128)}, u32[]{:S(2)}) copy-start(f32[64,256]{1,0:T(8,128)} %copy-done.8) | copy-start | bytes 196612
  111.6 25.1 %copy-start.11 = (f32[64,256]{1,0:T(8,128)S(1)}, f32[64,256]{1,0:T(8,128)}, u32[]{:S(2)}) copy-start(f32[64,256]{1,0:T(8,128)} %copy-done.10) | copy-start | bytes 196612
  112.0 8.6 %collective-permute-start.44 = (f32[64,256]{1,0:T(8,128)S(1)}, f32[64,256]{1,0:T(8,128)S(1)}, u32[]{:S(2)}, u32[]{:S(2)}) collective-permute-start(f32[64,256]{1,0:T(8,128)S(1)} %fusion.5), channel_id=1, source_target_pairs={{0,3},{1,2},{2,1},{3,0},{4,7},{5,6},{6,5},{7,4},{8,11},{9,10},{10,... | collective-permute-start | bytes 196616 | tf_op jit(solution)/shard_map/ppermute | solution.py:33
  114.7 4.9 %collective-permute-start.42 = (f32[64,256]{1,0:T(8,128)S(1)}, f32[64,256]{1,0:T(8,128)S(1)}, u32[]{:S(2)}, u32[]{:S(2)}) collective-permute-start(f32[64,256]{1,0:T(8,128)S(1)} %fusion.5), channel_id=1, source_target_pairs={{0,1},{1,0},{2,3},{3,2},{4,5},{5,4},{6,7},{7,6},{8,9},{9,8},{10,11... | collective-permute-start | bytes 196616 | tf_op jit(solution)/shard_map/ppermute | solution.py:33
  119.6 5.8 %collective-permute-start.43 = (f32[64,256]{1,0:T(8,128)S(1)}, f32[64,256]{1,0:T(8,128)S(1)}, u32[]{:S(2)}, u32[]{:S(2)}) collective-permute-start(f32[64,256]{1,0:T(8,128)S(1)} %fusion.5), channel_id=1, source_target_pairs={{0,2},{1,3},{2,0},{3,1},{4,6},{5,7},{6,4},{7,5},{8,10},{9,11},{10,... | collective-permute-start | bytes 196616 | tf_op jit(solution)/shard_map/ppermute | solution.py:33
  129.8 1.7 collective-permute-start.48
  133.2 4.5 %collective-permute-start.49 = (f32[2,16,512]{2,1,0:T(8,128)}, f32[2,16,512]{2,1,0:T(8,128)S(1)}, u32[]{:S(2)}, u32[]{:S(2)}) collective-permute-start(f32[2,16,512]{2,1,0:T(8,128)} %get-tuple-element.21), channel_id=1, source_target_pairs={{0,8},{4,12},{8,0},{12,4},{16,24},{20,28},{24,16},{28,20},{1,9},{5... | collective-permute-start | bytes 196616 | tf_op jit(solution)/shard_map/ppermute | solution.py:76
  134.7 4.5 %collective-permute-start.50 = (f32[2,16,512]{2,1,0:T(8,128)}, f32[2,16,512]{2,1,0:T(8,128)S(1)}, u32[]{:S(2)}, u32[]{:S(2)}) collective-permute-start(f32[2,16,512]{2,1,0:T(8,128)} %get-tuple-element.22), channel_id=1, source_target_pairs={{0,16},{4,20},{8,24},{12,28},{16,0},{20,4},{24,8},{28,12},{1,17},{... | collective-permute-start | bytes 196616 | tf_op jit(solution)/shard_map/ppermute | solution.py:76
  136.3 5.5 %collective-permute-start.51 = (f32[2,16,512]{2,1,0:T(8,128)}, f32[2,16,512]{2,1,0:T(8,128)}, u32[]{:S(2)}, u32[]{:S(2)}) collective-permute-start(f32[2,16,512]{2,1,0:T(8,128)} %get-tuple-element.23), channel_id=1, source_target_pairs={{0,24},{4,28},{8,16},{12,20},{16,8},{20,12},{24,0},{28,4},{1,25},{... | collective-permute-start | bytes 196616 | tf_op jit(solution)/shard_map/ppermute | solution.py:76
  143.8 9.7 %collective-permute-start.52 = (f32[16,1280]{1,0:T(8,128)}, f32[16,1280]{1,0:T(8,128)}, u32[]{:S(2)}, u32[]{:S(2)}) collective-permute-start(f32[16,1280]{1,0:T(8,128)} %get-tuple-element.25), channel_id=1, source_target_pairs={{0,1},{1,0},{2,3},{3,2},{4,5},{5,4},{6,7},{7,6},{8,9},{9,8},{10,11... | collective-permute-start | bytes 245768 | tf_op jit(solution)/shard_map/ppermute | solution.py:33
  143.8 9.7 %collective-permute-start.53 = (f32[16,1280]{1,0:T(8,128)}, f32[16,1280]{1,0:T(8,128)}, u32[]{:S(2)}, u32[]{:S(2)}) collective-permute-start(f32[16,1280]{1,0:T(8,128)} %get-tuple-element.26), channel_id=1, source_target_pairs={{0,2},{1,3},{2,0},{3,1},{4,6},{5,7},{6,4},{7,5},{8,10},{9,11},{10,... | collective-permute-start | bytes 245768 | tf_op jit(solution)/shard_map/ppermute | solution.py:33
  145.4 8.1 %collective-permute-start.54 = (f32[16,1280]{1,0:T(8,128)}, f32[16,1280]{1,0:T(8,128)}, u32[]{:S(2)}, u32[]{:S(2)}) collective-permute-start(f32[16,1280]{1,0:T(8,128)} %get-tuple-element.27), channel_id=1, source_target_pairs={{0,3},{1,2},{2,1},{3,0},{4,7},{5,6},{6,5},{7,4},{8,11},{9,10},{10,... | collective-permute-start | bytes 245768 | tf_op jit(solution)/shard_map/ppermute | solution.py:33
  156.4 5.9 %collective-permute-start.57 = (f32[16,256]{1,0:T(8,128)}, f32[16,256]{1,0:T(8,128)}, u32[]{:S(2)}, u32[]{:S(2)}) collective-permute-start(f32[16,256]{1,0:T(8,128)} %get-tuple-element.30.refs_0_), channel_id=1, source_target_pairs={{0,3},{1,2},{2,1},{3,0},{4,7},{5,6},{6,5},{7,4},{8,11},{9,10},{10,... | collective-permute-start | bytes 49160 | tf_op jit(solution)/shard_map/ppermute | solution.py:33
  157.6 5.0 %collective-permute-start.56 = (f32[16,256]{1,0:T(8,128)}, f32[16,256]{1,0:T(8,128)}, u32[]{:S(2)}, u32[]{:S(2)}) collective-permute-start(f32[16,256]{1,0:T(8,128)} %get-tuple-element.30.refs_0_), channel_id=1, source_target_pairs={{0,2},{1,3},{2,0},{3,1},{4,6},{5,7},{6,4},{7,5},{8,10},{9,11},{10,... | collective-permute-start | bytes 49160 | tf_op jit(solution)/shard_map/ppermute | solution.py:33
  158.0 4.9 %collective-permute-start.55 = (f32[16,256]{1,0:T(8,128)}, f32[16,256]{1,0:T(8,128)}, u32[]{:S(2)}, u32[]{:S(2)}) collective-permute-start(f32[16,256]{1,0:T(8,128)} %get-tuple-element.30.refs_0_), channel_id=1, source_target_pairs={{0,1},{1,0},{2,3},{3,2},{4,5},{5,4},{6,7},{7,6},{8,9},{9,8},{10,11... | collective-permute-start | bytes 49160 | tf_op jit(solution)/shard_map/ppermute | solution.py:33
  165.2 8.2 %collective-permute-start.60 = (f32[16,256]{1,0:T(8,128)}, f32[16,256]{1,0:T(8,128)S(1)}, u32[]{:S(2)}, u32[]{:S(2)}) collective-permute-start(f32[16,256]{1,0:T(8,128)} %shard_map.118.refs_0_), channel_id=1, source_target_pairs={{0,3},{1,2},{2,1},{3,0},{4,7},{5,6},{6,5},{7,4},{8,11},{9,10},{10,... | collective-permute-start | bytes 49160 | tf_op jit(solution)/shard_map/ppermute | solution.py:33
  167.6 5.9 %collective-permute-start.59 = (f32[16,256]{1,0:T(8,128)}, f32[16,256]{1,0:T(8,128)S(1)}, u32[]{:S(2)}, u32[]{:S(2)}) collective-permute-start(f32[16,256]{1,0:T(8,128)} %shard_map.118.refs_0_), channel_id=1, source_target_pairs={{0,2},{1,3},{2,0},{3,1},{4,6},{5,7},{6,4},{7,5},{8,10},{9,11},{10,... | collective-permute-start | bytes 49160 | tf_op jit(solution)/shard_map/ppermute | solution.py:33
  168.7 4.8 %collective-permute-start.58 = (f32[16,256]{1,0:T(8,128)}, f32[16,256]{1,0:T(8,128)S(1)}, u32[]{:S(2)}, u32[]{:S(2)}) collective-permute-start(f32[16,256]{1,0:T(8,128)} %shard_map.118.refs_0_), channel_id=1, source_target_pairs={{0,1},{1,0},{2,3},{3,2},{4,5},{5,4},{6,7},{7,6},{8,9},{9,8},{10,11... | collective-permute-start | bytes 49160 | tf_op jit(solution)/shard_map/ppermute | solution.py:33
  (20 other events, 285.8 us)

commit v9 on v8

--- a/solution.py
+++ b/solution.py
@@ -44,21 +44,6 @@
     return pieces
 
 
-def columns_of(factor, index, offset, width):
-    lead = factor.ndim - 3
-    begin = (0,) * lead + (index, 0, offset)
-    size = (1,) * (lead + 1) + (factor.shape[-2], width)
-    return lax.dynamic_slice(factor, begin, size).reshape(factor.shape[-2], width)
-
-
-def apply_rows(factor, index, pieces):
-    total = None
-    for offset, piece in pieces:
-        term = contract_last(piece, columns_of(factor, index, offset, piece.shape[1]))
-        total = term if total is None else total + term
-    return total
-
-
 def assemble(pieces, order):
     whole = jnp.zeros((pieces[0][1].shape[0], order), jnp.float32)
     for offset, piece in pieces:
@@ -89,6 +74,7 @@
         out_specs=[VMEM] * len(outs),
         scratch_shapes=list(scratch),
         cost_estimate=pl.CostEstimate(flops=flops, bytes_accessed=size, transcendentals=0),
+        compiler_params=pltpu.CompilerParams(vmem_limit_bytes=2 * size + 2**21),
     )(*operands)
 
 
@@ -117,32 +103,64 @@
     return groups // inner, inner
 
 
-def pack_terms(early, late, sources, blocks, count, last, tile_rows):
+def select_terms(sources_ref, gathered, tile_refs, store):
+    for m in range(tile_refs.shape[0]):
+        chosen = gathered[0][...]
+        for index in range(1, len(gathered)):
+            chosen = jnp.where(sources_ref[0, 0, m] == index, gathered[index][...], chosen)
+        top, rest = high_low(tile_refs[m])
+        store(m, split_product(chosen, top, rest))
+
+
+def tile_terms(gathered, tiles, sources):
+    slots, tile_rows, order = tiles.shape
+    depth = gathered[0].shape[0]
+    count = len(gathered)
+
+    def body(*refs):
+        out = refs[-1]
+
+        def store(m, term):
+            out[:, m * tile_rows : (m + 1) * tile_rows] = term
+
+        select_terms(refs[count + 1], refs[:count], refs[count], store)
+
+    return local_kernel(
+        body,
+        [float_array(depth, slots * tile_rows)],
+        [*gathered, tiles, sources],
+        [VMEM] * (count + 1) + [SMEM],
+        flops=6 * depth * slots * tile_rows * order,
+    )[0]
+
+
+def pack_terms(done, gathered, tiles, sources, blocks, live):
     outer, inner = leaf_shape()
-    slots = sources.shape[-1]
-    depth = early[0].shape[0]
-    streams = len(early)
+    slots, tile_rows, order = tiles.shape
+    depth = gathered[0].shape[0]
+    streams = len(done) + 1
     part = depth * streams // (outer * inner)
     width = (slots + 1) * tile_rows
-
-    def body(*refs):
-        early_refs, late_refs = refs[:streams], refs[streams : 2 * streams]
-        source_ref, block_ref, count_ref = refs[2 * streams : 2 * streams + 3]
-        outs = refs[2 * streams + 3 : -1]
+    count = len(gathered)
+    base = len(done)
+
+    def body(*refs):
+        source_ref, block_ref, live_ref = refs[base + count + 1 : base + count + 4]
+        outs = refs[base + count + 4 : -1]
         terms = refs[-1]
-        lanes = lax.broadcasted_iota(jnp.int32, (depth, tile_rows), 1)
-        tag = jnp.full((depth, tile_rows), -1.0, jnp.float32)
+        lanes = lax.broadcasted_iota(jnp.int32, (streams * depth, tile_rows), 1)
+        tag = jnp.full((streams * depth, tile_rows), -1.0, jnp.float32)
         for m in range(slots):
-            value = jnp.where(m < count_ref[0, 0], block_ref[0, 0, m], -1).astype(jnp.float32)
+            value = jnp.where(m < live_ref[0, 0], block_ref[0, 0, m], -1).astype(jnp.float32)
             tag = jnp.where(lanes == m, value, tag)
-        for i in range(streams):
-            rows = slice(i * depth, (i + 1) * depth)
-            for m in range(slots):
-                at = slice(m * tile_rows, (m + 1) * tile_rows)
-                terms[rows, at] = jnp.where(
-                    source_ref[0, 0, m] == last, late_refs[i][:, at], early_refs[i][:, at]
-                )
-            terms[rows, slots * tile_rows :] = tag
+        terms[:, slots * tile_rows :] = tag
+        for i in range(base):
+            terms[i * depth : (i + 1) * depth, : slots * tile_rows] = refs[i][...]
+
+        def store(m, term):
+            terms[base * depth :, m * tile_rows : (m + 1) * tile_rows] = term
+
+        select_terms(source_ref, refs[base : base + count], refs[base + count], store)
         inside = lax.rem(lax.axis_index("leaf"), inner)
         for o in range(outer):
             cut = [
@@ -155,10 +173,49 @@
     return local_kernel(
         body,
         [float_array(outer, part, width)] * inner,
-        [*early, *late, sources, blocks, count],
-        [VMEM] * (2 * streams) + [SMEM] * 3,
+        [*done, *gathered, tiles, sources, blocks, live],
+        [VMEM] * (base + count + 1) + [SMEM] * 3,
+        flops=6 * depth * slots * tile_rows * order,
         scratch=[pltpu.VMEM((streams * depth, width), jnp.float32)],
     )
+
+
+def turn(rhs, first, last, streams):
+    rows, count = rhs.shape[2:]
+    depth = count // streams
+
+    def body(rhs_ref, *outs):
+        for index in range(first, last):
+            wide = jnp.transpose(rhs_ref[0, index - first])
+            for i in range(streams):
+                outs[(index - first) * streams + i][...] = wide[i * depth : (i + 1) * depth]
+
+    return local_kernel(
+        body,
+        [float_array(depth, rows)] * (streams * (last - first)),
+        [rhs[:, first:last]],
+    )
+
+
+def turn_back(solved, after):
+    flat = [value for streams in solved for value in streams]
+    streams = len(solved[0])
+    depth, rows = flat[0].shape
+
+    def body(*refs):
+        out = refs[-1]
+        for index in range(len(solved)):
+            wide = jnp.concatenate(
+                [refs[index * streams + i][...] for i in range(streams)], axis=0
+            )
+            out[0, index] = jnp.transpose(wide)
+
+    return local_kernel(
+        body,
+        [float_array(1, len(solved), rows, depth * streams)],
+        [*flat, after],
+        [VMEM] * len(flat) + [pl.BlockSpec(memory_space=pl.ANY)],
+    )[0]
 
 
 def leaf_exchange(packed):
@@ -182,7 +239,7 @@
     ]
 
 
-def share_out(received, rhs_turned, order, slots, tile_rows):
+def share_out(received, rhs_turned, order, slots, tile_rows, after):
     members = lax.axis_size("grp")
     ancestors, part, rows = rhs_turned.shape
     inner = received[0].shape[0]
@@ -192,7 +249,7 @@
     def body(*refs):
         sources = refs[: len(received)]
         rhs_ref = refs[len(received)]
-        outs = refs[len(received) + 1 : -1]
+        outs = refs[len(received) + 2 : -1]
         share = refs[-1]
         me = lax.axis_index("grp")
         totals = [jnp.zeros((part, tile_rows), jnp.float32) for _ in range(block_count)]
@@ -224,7 +281,8 @@
     return local_kernel(
         body,
         [float_array(part, width)] * members,
-        [*received, rhs_turned],
+        [*received, rhs_turned, after],
+        [VMEM] * (len(received) + 1) + [pl.BlockSpec(memory_space=pl.ANY)],
         scratch=[pltpu.VMEM((part, ancestors * order), jnp.float32)],
     )
 
@@ -314,56 +372,38 @@
     diag_inv_anc,
     sub_anc,
 ):
-    rhs_group = rhs_local[0]
-    supernodes = rhs_group.shape[0]
-    order = diag_inv_local.shape[-1]
-    rhs_count = rhs_group.shape[-1]
+    supernodes, _, order = diag_inv_local.shape[1:]
+    rhs_count = rhs_local.shape[-1]
     members = lax.axis_size("grp")
     rows = order // members
-
-    tiles_mine = tiles[0, 0]
-    slots, tile_rows = tiles_mine.shape[:2]
-    sources = tile_source[0, 0]
+    slots, tile_rows = tiles.shape[2:4]
 
     streams = 2 if rhs_count % 16 == 0 else 1
-    depth = rhs_count // streams
-    first_rhs = jnp.transpose(lax.optimization_barrier(rhs_group[0]))
-    first_factor = lax.optimization_barrier(diag_inv_local[0, 0])
-    rhs_wide = jnp.swapaxes(rhs_group[1:], 1, 2)
-    split = [rhs_wide[:, i * depth : (i + 1) * depth] for i in range(streams)]
+    residuals = turn(rhs_local, 0, 1, streams)
+    later = turn(rhs_local, 1, supernodes, streams)
     solved = []
-    residuals = [first_rhs[i * depth : (i + 1) * depth] for i in range(streams)]
-    chosen = [jnp.zeros((slots, depth, order), jnp.float32) for _ in range(streams)]
+    gathered = []
     for current in range(supernodes):
-        factor, index = (diag_inv_local, current) if current else (first_factor[None], 0)
-        owned = [apply_rows(factor, index, gather_rows(r)) for r in residuals]
-        solved.append(jnp.transpose(jnp.concatenate(owned, axis=0)))
-        held = [gather_rows(value) for value in owned]
+        owned = []
+        for residual in residuals:
+            whole = assemble(gather_rows(residual), order)
+            owned.append(contract_last(whole, diag_inv_local[0, current]))
+        solved.append(owned)
+        gathered.append([assemble(gather_rows(value), order) for value in owned])
         if current + 1 < supernodes:
             residuals = [
-                portion[current] - apply_rows(sub_local, current, pieces)
-                for portion, pieces in zip(split, held)
+                later[current * streams + i] - contract_last(whole, sub_local[0, current])
+                for i, whole in enumerate(gathered[-1])
             ]
-            chosen = [
-                jnp.where((sources == current)[:, None, None], assemble(pieces, order)[None], old)
-                for pieces, old in zip(held, chosen)
-            ]
-
-    flat_tiles = tiles_mine.reshape(slots * tile_rows, order)
-    early = []
-    late = []
-    for pieces, picked in zip(held, chosen):
-        early.append(
-            jnp.concatenate(
-                [contract_last(picked[m], tiles_mine[m]) for m in range(slots)], axis=1
-            )
-        )
-        late.append(apply_rows(flat_tiles[None], 0, pieces))
-    packed = pack_terms(
-        early, late, tile_source, tile_block, tile_count, supernodes - 1, tile_rows
-    )
+
+    by_stream = [[values[i] for values in gathered] for i in range(streams)]
+    done = [tile_terms(values, tiles[0, 0], tile_source) for values in by_stream[:-1]]
+    packed = pack_terms(done, by_stream[-1], tiles[0, 0], tile_source, tile_block, tile_count)
     received = leaf_exchange(packed)
-    shares = share_out(received, jnp.swapaxes(rhs_anc, 1, 2), order, slots, tile_rows)
+    solution_local = turn_back(solved, packed[0])
+    shares = share_out(
+        received, jnp.swapaxes(rhs_anc, 1, 2), order, slots, tile_rows, solution_local
+    )
     payloads = [shares[0]] + [send(shares[d], "grp", d) for d in range(1, members)]
     inverse_top, inverse_rest, below_top, below_rest = split_factors(
         [diag_inv_anc, sub_anc], shares[0]
@@ -378,7 +418,7 @@
         pieces = [piece for _, piece in gather_rows(residual)]
         solutions.append(apply_split(pieces, inverse_top, inverse_rest, ancestor))
     solutions = jnp.swapaxes(jnp.stack(solutions), 1, 2)
-    return (jnp.stack(solved)[None], solutions)
+    return (solution_local, solutions)
 
 
 def solution(mesh):

time: 180 us -> 164 us (0.911)
  waiting for transfers between devices: 21.3 us -> 47.8 us
  matrix products: 31.9 us -> 11.4 us
  Pallas kernels: 17.3 us -> 6.86 us
  other arithmetic: 7.7 us -> 0.65 us
  local copies, waits for them, and re-layouts: 9.7 us -> 3.83 us
  starting transfers between devices: 88.5 us -> 91.5 us
    ppermute x57, waiting for transfers between devices: 15.9 us -> 42.8 us  [send(): return lax.ppermute(value, axis, pairs)]
    dot_general x70 -> x14, matrix products: 31.9 us -> 11.4 us  [contract_last(): lax.dot_general(left, right, (((left.ndim - 1,), (right.ndim - 1,)), ((),...]
    pallas_call x7 -> x11, Pallas kernels: 17.3 us -> 6.86 us  [local_kernel(): pl.pallas_call(body, out_shape=list(outs), in_specs=specs or [VMEM] * len...]
    another operation x4 -> x0, other arithmetic: 3.51 us -> none  [on_device(): return (jnp.stack(solved)[None], solutions)]
    squeeze x2 -> x0, local copies, waits for them, and re-layouts: 3.37 us -> none  [the longest x1 2.3 us: on_device(): first_factor = lax.optimization_barrier(diag_inv_local[0, 0])]
    unnamed x48 -> x18, local copies, waits for them, and re-layouts: 4.22 us -> 1.09 us
    ppermute x57, starting transfers between devices: 85 us -> 87.9 us  [send(): return lax.ppermute(value, axis, pairs)]
    broadcast_in_dim x1 -> x0, other arithmetic: 1.81 us -> none  [on_device(): return (jnp.stack(solved)[None], solutions)]
  transfers between devices with their start and end apart: 61 -> 61, of which waited for: 12 -> 20; matrix products, arithmetic and copies ran while one was open for 25% -> 8% of each run, Pallas kernels for 2% -> 2%
where the time goes in v9:
time: 164 us
  starting transfers between devices  91.5 us (56%)
  waiting for transfers between devices  47.8 us (29%)
  matrix products  11.4 us (7%)
  Pallas kernels  6.86 us (4%)
  local copies, waits for them, and re-layouts  3.83 us (2%)
  between operations  2.14 us (1%)
    ppermute x57, starting transfers between devices, send(): return lax.ppermute(value, axis, pairs)  87.9 us
    ppermute x57, waiting for transfers between devices, send(): return lax.ppermute(value, axis, pairs)  42.8 us
    dot_general x14, matrix products, contract_last(): lax.dot_general(left, right, (((left.ndim - 1,), (right.ndim - 1,)), ((),...  11.4 us
    pallas_call x11, Pallas kernels, local_kernel(): pl.pallas_call(body, out_shape=list(outs), in_specs=specs or [VMEM] * len...  6.86 us
    ppermute x3, waiting for transfers between devices, swap(): return lax.ppermute(value, axis, pairs)  3.65 us
    ppermute x3, starting transfers between devices, swap(): return lax.ppermute(value, axis, pairs)  3.55 us
  transfers between devices with their start and end apart: 61, of which 20 were waited for; matrix products, arithmetic and copies ran while one was open for 8% of the time, Pallas kernels for 2%

profile of v9, /device:TPU:0, one launch (start us, length us, event | category | flops | bytes accessed | tf_op | source)
XLA Modules:
  0.0 164.2 jit_solution(4171937434341248138)
XLA Ops:
  1.7 3.1 %collective-permute-start = (f32[64,256]{1,0:T(8,128)S(1)}, f32[64,256]{1,0:T(8,128)S(1)}, u32[]{:S(2)}, u32[]{:S(2)}) collective-permute-start(f32[64,256]{1,0:T(8,128)S(1)} %get-tuple-element.26), channel_id=1, source_target_pairs={{0,1},{1,0},{2,3},{3,2},{4,5},{5,4},{6,7},{7,6},{8,9},{9,8},{10,11... | collective-permute-start | bytes 196616 | tf_op jit(solution)/shard_map/ppermute | solution.py:33
  4.7 2.6 %collective-permute-start.1 = (f32[64,256]{1,0:T(8,128)S(1)}, f32[64,256]{1,0:T(8,128)S(1)}, u32[]{:S(2)}, u32[]{:S(2)}) collective-permute-start(f32[64,256]{1,0:T(8,128)S(1)} %get-tuple-element.26), channel_id=1, source_target_pairs={{0,2},{1,3},{2,0},{3,1},{4,6},{5,7},{6,4},{7,5},{8,10},{9,11},{10,... | collective-permute-start | bytes 196616 | tf_op jit(solution)/shard_map/ppermute | solution.py:33
  8.2 3.5 %collective-permute-start.4 = (f32[64,256]{1,0:T(8,128)S(1)}, f32[64,256]{1,0:T(8,128)S(1)}, u32[]{:S(2)}, u32[]{:S(2)}) collective-permute-start(f32[64,256]{1,0:T(8,128)S(1)} %get-tuple-element.27), channel_id=1, source_target_pairs={{0,2},{1,3},{2,0},{3,1},{4,6},{5,7},{6,4},{7,5},{8,10},{9,11},{10,... | collective-permute-start | bytes 196616 | tf_op jit(solution)/shard_map/ppermute | solution.py:33
  13.7 2.5 %collective-permute-start.5 = (f32[64,256]{1,0:T(8,128)S(1)}, f32[64,256]{1,0:T(8,128)S(1)}, u32[]{:S(2)}, u32[]{:S(2)}) collective-permute-start(f32[64,256]{1,0:T(8,128)S(1)} %get-tuple-element.27), channel_id=1, source_target_pairs={{0,3},{1,2},{2,1},{3,0},{4,7},{5,6},{6,5},{7,4},{8,11},{9,10},{10,... | collective-permute-start | bytes 196616 | tf_op jit(solution)/shard_map/ppermute | solution.py:33
  16.2 1.4 collective-permute-done.4
  17.6 2.2 %collective-permute-done.5 = f32[64,256]{1,0:T(8,128)S(1)} collective-permute-done((f32[64,256]{1,0:T(8,128)S(1)}, f32[64,256]{1,0:T(8,128)S(1)}, u32[]{:S(2)}, u32[]{:S(2)}) %collective-permute-start.5) | collective-permute-done | bytes 65568 | tf_op jit(solution)/shard_map/ppermute | solution.py:33
  19.9 2.0 %constant_dynamic-update-slice_fusion.47 = (f32[64,1024]{1,0:T(8,128)S(1)}, f32[64,256]{1,0:T(8,128)S(1)}) fusion(f32[64,1024]{1,0:T(8,128)S(1)} %broadcast.3.clone.2, s32[]{:T(128)S(6)} %select_n.8, f32[64,1024]{1,0:T(8,128)S(1)} %constant_dynamic-update-slice_fusion.56, f32[1,4,256,1024]{3,2,1,0:T(8,128)} %param.11), kind=kOutput, calls=%fused_computation.90 | convolution fusion | flops 100663296 | bytes 1441796 | tf_op jit(solution)/shard_map/dot_general | solution.py:12
  22.1 1.8 %constant_dynamic-update-slice_fusion.55 = (f32[64,1024]{1,0:T(8,128)S(1)}, f32[64,256]{1,0:T(8,128)S(1)}) fusion(f32[64,1024]{1,0:T(8,128)S(1)} %broadcast.3.clone, s32[]{:T(128)S(6)} %select_n.8, f32[64,1024]{1,0:T(8,128)S(1)} %constant_dynamic-update-slice_fusion.60, f32[1,4,256,1024]{3,2,1,0:T(8,128)} %param.11), kind=kOutput, calls=%fused_computation.98 | convolution fusion | flops 100663296 | bytes 1441796 | tf_op jit(solution)/shard_map/dot_general | solution.py:12
  23.9 2.1 %collective-permute-start.6 = (f32[64,256]{1,0:T(8,128)S(1)}, f32[64,256]{1,0:T(8,128)S(1)}, u32[]{:S(2)}, u32[]{:S(2)}) collective-permute-start(f32[64,256]{1,0:T(8,128)S(1)} %get-tuple-element.51.refs_0_), channel_id=1, source_target_pairs={{0,1},{1,0},{2,3},{3,2},{4,5},{5,4},{6,7},{7,6},{8,9},{9,8},{10,11... | collective-permute-start | bytes 196616 | tf_op jit(solution)/shard_map/ppermute | solution.py:33
  26.0 1.1 collective-permute-start.7
  27.1 1.4 collective-permute-start.8
  28.4 2.0 %collective-permute-start.13 = (f32[64,256]{1,0:T(8,128)S(1)}, f32[64,256]{1,0:T(8,128)S(1)}, u32[]{:S(2)}, u32[]{:S(2)}) collective-permute-start(f32[64,256]{1,0:T(8,128)S(1)} %get-tuple-element.55.refs_1_), channel_id=1, source_target_pairs={{0,2},{1,3},{2,0},{3,1},{4,6},{5,7},{6,4},{7,5},{8,10},{9,11},{10,... | collective-permute-start | bytes 196616 | tf_op jit(solution)/shard_map/ppermute | solution.py:33
  30.5 1.4 collective-permute-start.14
  31.8 5.0 %collective-permute-done.13 = f32[64,256]{1,0:T(8,128)S(1)} collective-permute-done((f32[64,256]{1,0:T(8,128)S(1)}, f32[64,256]{1,0:T(8,128)S(1)}, u32[]{:S(2)}, u32[]{:S(2)}) %collective-permute-start.13) | collective-permute-done | bytes 65568 | tf_op jit(solution)/shard_map/ppermute | solution.py:33
  37.5 1.3 collective-permute-start.15
  40.4 1.5 collective-permute-start.10
  41.9 2.1 %collective-permute-start.11 = (f32[64,256]{1,0:T(8,128)S(1)}, f32[64,256]{1,0:T(8,128)S(1)}, u32[]{:S(2)}, u32[]{:S(2)}) collective-permute-start(f32[64,256]{1,0:T(8,128)S(1)} %get-tuple-element.53), channel_id=1, source_target_pairs={{0,3},{1,2},{2,1},{3,0},{4,7},{5,6},{6,5},{7,4},{8,11},{9,10},{10,... | collective-permute-start | bytes 196616 | tf_op jit(solution)/shard_map/ppermute | solution.py:33
  44.3 2.0 %collective-permute-start.17 = (f32[64,256]{1,0:T(8,128)S(1)}, f32[64,256]{1,0:T(8,128)S(1)}, u32[]{:S(2)}, u32[]{:S(2)}) collective-permute-start(f32[64,256]{1,0:T(8,128)S(1)} %get-tuple-element.57), channel_id=1, source_target_pairs={{0,3},{1,2},{2,1},{3,0},{4,7},{5,6},{6,5},{7,4},{8,11},{9,10},{10,... | collective-permute-start | bytes 196616 | tf_op jit(solution)/shard_map/ppermute | solution.py:33
  46.3 5.2 %collective-permute-done.16 = f32[64,256]{1,0:T(8,128)S(1)} collective-permute-done((f32[64,256]{1,0:T(8,128)S(1)}, f32[64,256]{1,0:T(8,128)S(1)}, u32[]{:S(2)}, u32[]{:S(2)}) %collective-permute-start.16) | collective-permute-done | bytes 65568 | tf_op jit(solution)/shard_map/ppermute | solution.py:33
  52.2 1.3 collective-permute-start.24
  55.1 1.6 collective-permute-start.19
  56.7 2.0 %collective-permute-start.20 = (f32[64,256]{1,0:T(8,128)S(1)}, f32[64,256]{1,0:T(8,128)S(1)}, u32[]{:S(2)}, u32[]{:S(2)}) collective-permute-start(f32[64,256]{1,0:T(8,128)S(1)} %get-tuple-element.59.refs_2_), channel_id=1, source_target_pairs={{0,3},{1,2},{2,1},{3,0},{4,7},{5,6},{6,5},{7,4},{8,11},{9,10},{10,... | collective-permute-start | bytes 196616 | tf_op jit(solution)/shard_map/ppermute | solution.py:33
  59.0 2.0 %collective-permute-start.26 = (f32[64,256]{1,0:T(8,128)S(1)}, f32[64,256]{1,0:T(8,128)S(1)}, u32[]{:S(2)}, u32[]{:S(2)}) collective-permute-start(f32[64,256]{1,0:T(8,128)S(1)} %get-tuple-element.63.refs_3_), channel_id=1, source_target_pairs={{0,3},{1,2},{2,1},{3,0},{4,7},{5,6},{6,5},{7,4},{8,11},{9,10},{10,... | collective-permute-start | bytes 196616 | tf_op jit(solution)/shard_map/ppermute | solution.py:33
  61.0 5.2 %collective-permute-done.25 = f32[64,256]{1,0:T(8,128)S(1)} collective-permute-done((f32[64,256]{1,0:T(8,128)S(1)}, f32[64,256]{1,0:T(8,128)S(1)}, u32[]{:S(2)}, u32[]{:S(2)}) %collective-permute-start.25) | collective-permute-done | bytes 65568 | tf_op jit(solution)/shard_map/ppermute | solution.py:33
  66.9 1.3 collective-permute-start.27
  69.8 1.8 %collective-permute-start.22 = (f32[64,256]{1,0:T(8,128)S(1)}, f32[64,256]{1,0:T(8,128)S(1)}, u32[]{:S(2)}, u32[]{:S(2)}) collective-permute-start(f32[64,256]{1,0:T(8,128)S(1)} %get-tuple-element.61), channel_id=1, source_target_pairs={{0,2},{1,3},{2,0},{3,1},{4,6},{5,7},{6,4},{7,5},{8,10},{9,11},{10,... | collective-permute-start | bytes 196616 | tf_op jit(solution)/shard_map/ppermute | solution.py:33
  71.6 1.8 %collective-permute-start.23 = (f32[64,256]{1,0:T(8,128)S(1)}, f32[64,256]{1,0:T(8,128)S(1)}, u32[]{:S(2)}, u32[]{:S(2)}) collective-permute-start(f32[64,256]{1,0:T(8,128)S(1)} %get-tuple-element.61), channel_id=1, source_target_pairs={{0,3},{1,2},{2,1},{3,0},{4,7},{5,6},{6,5},{7,4},{8,11},{9,10},{10,... | collective-permute-start | bytes 196616 | tf_op jit(solution)/shard_map/ppermute | solution.py:33
  73.9 1.8 %collective-permute-start.29 = (f32[64,256]{1,0:T(8,128)S(1)}, f32[64,256]{1,0:T(8,128)S(1)}, u32[]{:S(2)}, u32[]{:S(2)}) collective-permute-start(f32[64,256]{1,0:T(8,128)S(1)} %get-tuple-element.65), channel_id=1, source_target_pairs={{0,3},{1,2},{2,1},{3,0},{4,7},{5,6},{6,5},{7,4},{8,11},{9,10},{10,... | collective-permute-start | bytes 196616 | tf_op jit(solution)/shard_map/ppermute | solution.py:33
  75.6 5.4 %collective-permute-done.28 = f32[64,256]{1,0:T(8,128)S(1)} collective-permute-done((f32[64,256]{1,0:T(8,128)S(1)}, f32[64,256]{1,0:T(8,128)S(1)}, u32[]{:S(2)}, u32[]{:S(2)}) %collective-permute-start.28) | collective-permute-done | bytes 65568 | tf_op jit(solution)/shard_map/ppermute | solution.py:33
  81.7 1.3 collective-permute-start.36
  83.0 1.3 collective-permute-start.37
  84.4 1.8 %collective-permute-start.38 = (f32[64,256]{1,0:T(8,128)S(1)}, f32[64,256]{1,0:T(8,128)S(1)}, u32[]{:S(2)}, u32[]{:S(2)}) collective-permute-start(f32[64,256]{1,0:T(8,128)S(1)} %get-tuple-element.71.refs_5_), channel_id=1, source_target_pairs={{0,3},{1,2},{2,1},{3,0},{4,7},{5,6},{6,5},{7,4},{8,11},{9,10},{10,... | collective-permute-start | bytes 196616 | tf_op jit(solution)/shard_map/ppermute | solution.py:33
  87.3 2.2 %collective-permute-start.31 = (f32[64,256]{1,0:T(8,128)S(1)}, f32[64,256]{1,0:T(8,128)S(1)}, u32[]{:S(2)}, u32[]{:S(2)}) collective-permute-start(f32[64,256]{1,0:T(8,128)S(1)} %get-tuple-element.67.refs_4_), channel_id=1, source_target_pairs={{0,2},{1,3},{2,0},{3,1},{4,6},{5,7},{6,4},{7,5},{8,10},{9,11},{10,... | collective-permute-start | bytes 196616 | tf_op jit(solution)/shard_map/ppermute | solution.py:33
  89.5 1.9 %collective-permute-start.32 = (f32[64,256]{1,0:T(8,128)S(1)}, f32[64,256]{1,0:T(8,128)S(1)}, u32[]{:S(2)}, u32[]{:S(2)}) collective-permute-start(f32[64,256]{1,0:T(8,128)S(1)} %get-tuple-element.67.refs_4_), channel_id=1, source_target_pairs={{0,3},{1,2},{2,1},{3,0},{4,7},{5,6},{6,5},{7,4},{8,11},{9,10},{10,... | collective-permute-start | bytes 196616 | tf_op jit(solution)/shard_map/ppermute | solution.py:33
  92.4 4.8 %collective-permute-start.39 = (f32[64,256]{1,0:T(8,128)S(1)}, f32[64,256]{1,0:T(8,128)S(1)}, u32[]{:S(2)}, u32[]{:S(2)}) collective-permute-start(f32[64,256]{1,0:T(8,128)S(1)} %get-tuple-element.73), channel_id=1, source_target_pairs={{0,1},{1,0},{2,3},{3,2},{4,5},{5,4},{6,7},{7,6},{8,9},{9,8},{10,11... | collective-permute-start | bytes 196616 | tf_op jit(solution)/shard_map/ppermute | solution.py:33
  97.8 1.8 %collective-permute-start.41 = (f32[64,256]{1,0:T(8,128)S(1)}, f32[64,256]{1,0:T(8,128)S(1)}, u32[]{:S(2)}, u32[]{:S(2)}) collective-permute-start(f32[64,256]{1,0:T(8,128)S(1)} %get-tuple-element.73), channel_id=1, source_target_pairs={{0,3},{1,2},{2,1},{3,0},{4,7},{5,6},{6,5},{7,4},{8,11},{9,10},{10,... | collective-permute-start | bytes 196616 | tf_op jit(solution)/shard_map/ppermute | solution.py:33
  100.4 1.1 collective-permute-start.33
  101.5 1.5 collective-permute-start.34
  103.0 1.8 %collective-permute-start.35 = (f32[64,256]{1,0:T(8,128)S(1)}, f32[64,256]{1,0:T(8,128)S(1)}, u32[]{:S(2)}, u32[]{:S(2)}) collective-permute-start(f32[64,256]{1,0:T(8,128)S(1)} %get-tuple-element.69), channel_id=1, source_target_pairs={{0,3},{1,2},{2,1},{3,0},{4,7},{5,6},{6,5},{7,4},{8,11},{9,10},{10,... | collective-permute-start | bytes 196616 | tf_op jit(solution)/shard_map/ppermute | solution.py:33
  105.0 3.3 %collective-permute-done.34 = f32[64,256]{1,0:T(8,128)S(1)} collective-permute-done((f32[64,256]{1,0:T(8,128)S(1)}, f32[64,256]{1,0:T(8,128)S(1)}, u32[]{:S(2)}, u32[]{:S(2)}) %collective-permute-start.34) | collective-permute-done | bytes 65568 | tf_op jit(solution)/shard_map/ppermute | solution.py:33
  109.9 2.5 %collective-permute-start.42 = (f32[64,256]{1,0:T(8,128)S(1)}, f32[64,256]{1,0:T(8,128)S(1)}, u32[]{:S(2)}, u32[]{:S(2)}) collective-permute-start(f32[64,256]{1,0:T(8,128)S(1)} %get-tuple-element.75.refs_6_), channel_id=1, source_target_pairs={{0,1},{1,0},{2,3},{3,2},{4,5},{5,4},{6,7},{7,6},{8,9},{9,8},{10,11... | collective-permute-start | bytes 196616 | tf_op jit(solution)/shard_map/ppermute | solution.py:33
  113.3 1.5 collective-permute-start.44
  115.5 1.1 collective-permute-start.45
  116.6 1.8 %collective-permute-start.46 = (f32[64,256]{1,0:T(8,128)S(1)}, f32[64,256]{1,0:T(8,128)S(1)}, u32[]{:S(2)}, u32[]{:S(2)}) collective-permute-start(f32[64,256]{1,0:T(8,128)S(1)} %get-tuple-element.77.refs_7_), channel_id=1, source_target_pairs={{0,2},{1,3},{2,0},{3,1},{4,6},{5,7},{6,4},{7,5},{8,10},{9,11},{10,... | collective-permute-start | bytes 196616 | tf_op jit(solution)/shard_map/ppermute | solution.py:33
  118.4 1.5 collective-permute-start.47
  120.0 1.5 shard_map.115.refs_0_
  122.5 2.0 %collective-permute-done.47 = f32[64,256]{1,0:T(8,128)S(1)} collective-permute-done((f32[64,256]{1,0:T(8,128)S(1)}, f32[64,256]{1,0:T(8,128)S(1)}, u32[]{:S(2)}, u32[]{:S(2)}) %collective-permute-start.47) | collective-permute-done | bytes 65568 | tf_op jit(solution)/shard_map/ppermute | solution.py:33
  124.5 1.7 %shard_map.116 = (f32[4,16,512]{2,1,0:T(8,128)S(1)}, f32[4,16,512]{2,1,0:T(8,128)S(1)}) custom-call(f32[64,384]{1,0:T(8,128)S(1)} %shard_map.115.refs_0_, f32[64,1024]{1,0:T(8,128)S(1)} %constant_dynamic-update-slice_fusion.44.refs_1_, f32[64,1024]{1,0:T(8,128)S(1)} %constant_dynamic-update-slice_fusion.28.refs_2_, ...), custom_call_target="tpu_custom_call" | custom-call | flops 150994944 | bytes 2981916 | tf_op jit(solution)/shard_map/pallas_call | solution.py:70
  126.3 1.3 collective-permute-done.48.refs_1_
  127.6 1.5 collective-permute-start.49
  129.2 1.5 collective-permute-start.50
  132.2 1.2 collective-permute-done.50.refs_2_
  133.4 2.4 %collective-permute-done.51.refs_3_ = f32[2,16,512]{2,1,0:T(8,128)S(1)} collective-permute-done((f32[2,16,512]{2,1,0:T(8,128)S(1)}, f32[2,16,512]{2,1,0:T(8,128)S(1)}, u32[]{:S(2)}, u32[]{:S(2)}) %collective-permute-start.51) | collective-permute-done | bytes 65568 | tf_op jit(solution)/shard_map/ppermute | solution.py:61
  137.4 2.2 %collective-permute-start.53 = (f32[16,1280]{1,0:T(8,128)S(1)}, f32[16,1280]{1,0:T(8,128)S(1)}, u32[]{:S(2)}, u32[]{:S(2)}) collective-permute-start(f32[16,1280]{1,0:T(8,128)S(1)} %get-tuple-element.42), channel_id=1, source_target_pairs={{0,2},{1,3},{2,0},{3,1},{4,6},{5,7},{6,4},{7,5},{8,10},{9,11},{10,... | collective-permute-start | bytes 245768 | tf_op jit(solution)/shard_map/ppermute | solution.py:33
  139.6 2.1 %collective-permute-start.54 = (f32[16,1280]{1,0:T(8,128)S(1)}, f32[16,1280]{1,0:T(8,128)S(1)}, u32[]{:S(2)}, u32[]{:S(2)}) collective-permute-start(f32[16,1280]{1,0:T(8,128)S(1)} %get-tuple-element.43), channel_id=1, source_target_pairs={{0,3},{1,2},{2,1},{3,0},{4,7},{5,6},{6,5},{7,4},{8,11},{9,10},{10,... | collective-permute-start | bytes 245768 | tf_op jit(solution)/shard_map/ppermute | solution.py:33
  142.2 2.4 %collective-permute-done.53.refs_2_ = f32[16,1280]{1,0:T(8,128)S(1)} collective-permute-done((f32[16,1280]{1,0:T(8,128)S(1)}, f32[16,1280]{1,0:T(8,128)S(1)}, u32[]{:S(2)}, u32[]{:S(2)}) %collective-permute-start.53) | collective-permute-done | bytes 81952 | tf_op jit(solution)/shard_map/ppermute | solution.py:33
  144.6 1.3 collective-permute-done.54.refs_3_
  147.5 1.7 %collective-permute-start.56 = (f32[16,256]{1,0:T(8,128)S(1)}, f32[16,256]{1,0:T(8,128)S(1)}, u32[]{:S(2)}, u32[]{:S(2)}) collective-permute-start(f32[16,256]{1,0:T(8,128)S(1)} %get-tuple-element.46.refs_0_), channel_id=1, source_target_pairs={{0,2},{1,3},{2,0},{3,1},{4,6},{5,7},{6,4},{7,5},{8,10},{9,11},{10,... | collective-permute-start | bytes 49160 | tf_op jit(solution)/shard_map/ppermute | solution.py:33
  149.2 1.7 %collective-permute-start.57 = (f32[16,256]{1,0:T(8,128)S(1)}, f32[16,256]{1,0:T(8,128)S(1)}, u32[]{:S(2)}, u32[]{:S(2)}) collective-permute-start(f32[16,256]{1,0:T(8,128)S(1)} %get-tuple-element.46.refs_0_), channel_id=1, source_target_pairs={{0,3},{1,2},{2,1},{3,0},{4,7},{5,6},{6,5},{7,4},{8,11},{9,10},{10,... | collective-permute-start | bytes 49160 | tf_op jit(solution)/shard_map/ppermute | solution.py:33
  150.9 1.3 collective-permute-done.56.refs_2_
  152.1 2.7 %collective-permute-done.57.refs_3_ = f32[16,256]{1,0:T(8,128)S(1)} collective-permute-done((f32[16,256]{1,0:T(8,128)S(1)}, f32[16,256]{1,0:T(8,128)S(1)}, u32[]{:S(2)}, u32[]{:S(2)}) %collective-permute-start.57) | collective-permute-done | bytes 16416 | tf_op jit(solution)/shard_map/ppermute | solution.py:33
  155.3 2.2 %collective-permute-start.59 = (f32[16,256]{1,0:T(8,128)S(1)}, f32[16,256]{1,0:T(8,128)S(1)}, u32[]{:S(2)}, u32[]{:S(2)}) collective-permute-start(f32[16,256]{1,0:T(8,128)S(1)} %shard_map.122.refs_0_), channel_id=1, source_target_pairs={{0,2},{1,3},{2,0},{3,1},{4,6},{5,7},{6,4},{7,5},{8,10},{9,11},{10,... | collective-permute-start | bytes 49160 | tf_op jit(solution)/shard_map/ppermute | solution.py:33
  157.5 2.3 %collective-permute-start.60 = (f32[16,256]{1,0:T(8,128)S(1)}, f32[16,256]{1,0:T(8,128)S(1)}, u32[]{:S(2)}, u32[]{:S(2)}) collective-permute-start(f32[16,256]{1,0:T(8,128)S(1)} %shard_map.122.refs_0_), channel_id=1, source_target_pairs={{0,3},{1,2},{2,1},{3,0},{4,7},{5,6},{6,5},{7,4},{8,11},{9,10},{10,... | collective-permute-start | bytes 49160 | tf_op jit(solution)/shard_map/ppermute | solution.py:33
  160.0 3.0 %collective-permute-done.60.refs_3_ = f32[16,256]{1,0:T(8,128)S(1)} collective-permute-done((f32[16,256]{1,0:T(8,128)S(1)}, f32[16,256]{1,0:T(8,128)S(1)}, u32[]{:S(2)}, u32[]{:S(2)}) %collective-permute-start.60) | collective-permute-done | bytes 16416 | tf_op jit(solution)/shard_map/ppermute | solution.py:33
  (169 shorter events, 26.3 us)
Async XLA Ops:
  1.7 20.3 %collective-permute-start = (f32[64,256]{1,0:T(8,128)S(1)}, f32[64,256]{1,0:T(8,128)S(1)}, u32[]{:S(2)}, u32[]{:S(2)}) collective-permute-start(f32[64,256]{1,0:T(8,128)S(1)} %get-tuple-element.26), channel_id=1, source_target_pairs={{0,1},{1,0},{2,3},{3,2},{4,5},{5,4},{6,7},{7,6},{8,9},{9,8},{10,11... | collective-permute-start | bytes 196616 | tf_op jit(solution)/shard_map/ppermute | solution.py:33
  4.7 17.2 %collective-permute-start.1 = (f32[64,256]{1,0:T(8,128)S(1)}, f32[64,256]{1,0:T(8,128)S(1)}, u32[]{:S(2)}, u32[]{:S(2)}) collective-permute-start(f32[64,256]{1,0:T(8,128)S(1)} %get-tuple-element.26), channel_id=1, source_target_pairs={{0,2},{1,3},{2,0},{3,1},{4,6},{5,7},{6,4},{7,5},{8,10},{9,11},{10,... | collective-permute-start | bytes 196616 | tf_op jit(solution)/shard_map/ppermute | solution.py:33
  7.3 14.7 %collective-permute-start.2 = (f32[64,256]{1,0:T(8,128)S(1)}, f32[64,256]{1,0:T(8,128)S(1)}, u32[]{:S(2)}, u32[]{:S(2)}) collective-permute-start(f32[64,256]{1,0:T(8,128)S(1)} %get-tuple-element.26), channel_id=1, source_target_pairs={{0,3},{1,2},{2,1},{3,0},{4,7},{5,6},{6,5},{7,4},{8,11},{9,10},{10,... | collective-permute-start | bytes 196616 | tf_op jit(solution)/shard_map/ppermute | solution.py:33
  7.3 6.4 %collective-permute-start.3 = (f32[64,256]{1,0:T(8,128)S(1)}, f32[64,256]{1,0:T(8,128)S(1)}, u32[]{:S(2)}, u32[]{:S(2)}) collective-permute-start(f32[64,256]{1,0:T(8,128)S(1)} %get-tuple-element.27), channel_id=1, source_target_pairs={{0,1},{1,0},{2,3},{3,2},{4,5},{5,4},{6,7},{7,6},{8,9},{9,8},{10,11... | collective-permute-start | bytes 196616 | tf_op jit(solution)/shard_map/ppermute | solution.py:33
  8.2 9.4 %collective-permute-start.4 = (f32[64,256]{1,0:T(8,128)S(1)}, f32[64,256]{1,0:T(8,128)S(1)}, u32[]{:S(2)}, u32[]{:S(2)}) collective-permute-start(f32[64,256]{1,0:T(8,128)S(1)} %get-tuple-element.27), channel_id=1, source_target_pairs={{0,2},{1,3},{2,0},{3,1},{4,6},{5,7},{6,4},{7,5},{8,10},{9,11},{10,... | collective-permute-start | bytes 196616 | tf_op jit(solution)/shard_map/ppermute | solution.py:33
  13.7 6.1 %collective-permute-start.5 = (f32[64,256]{1,0:T(8,128)S(1)}, f32[64,256]{1,0:T(8,128)S(1)}, u32[]{:S(2)}, u32[]{:S(2)}) collective-permute-start(f32[64,256]{1,0:T(8,128)S(1)} %get-tuple-element.27), channel_id=1, source_target_pairs={{0,3},{1,2},{2,1},{3,0},{4,7},{5,6},{6,5},{7,4},{8,11},{9,10},{10,... | collective-permute-start | bytes 196616 | tf_op jit(solution)/shard_map/ppermute | solution.py:33
  19.9 31.7 %copy-start.7 = (f32[1,4,256,1024]{3,2,1,0:T(8,128)S(1)}, f32[1,4,256,1024]{3,2,1,0:T(8,128)}, u32[]{:S(2)}) copy-start(f32[1,4,256,1024]{3,2,1,0:T(8,128)} %param.11) | copy-start | bytes 12582916
  21.9 8.6 %collective-permute-start.12 = (f32[64,256]{1,0:T(8,128)S(1)}, f32[64,256]{1,0:T(8,128)S(1)}, u32[]{:S(2)}, u32[]{:S(2)}) collective-permute-start(f32[64,256]{1,0:T(8,128)S(1)} %get-tuple-element.55.refs_1_), channel_id=1, source_target_pairs={{0,1},{1,0},{2,3},{3,2},{4,5},{5,4},{6,7},{7,6},{8,9},{9,8},{10,11... | collective-permute-start | bytes 196616 | tf_op jit(solution)/shard_map/ppermute | solution.py:33
  23.9 14.9 %collective-permute-start.6 = (f32[64,256]{1,0:T(8,128)S(1)}, f32[64,256]{1,0:T(8,128)S(1)}, u32[]{:S(2)}, u32[]{:S(2)}) collective-permute-start(f32[64,256]{1,0:T(8,128)S(1)} %get-tuple-element.51.refs_0_), channel_id=1, source_target_pairs={{0,1},{1,0},{2,3},{3,2},{4,5},{5,4},{6,7},{7,6},{8,9},{9,8},{10,11... | collective-permute-start | bytes 196616 | tf_op jit(solution)/shard_map/ppermute | solution.py:33
  26.0 12.9 %collective-permute-start.7 = (f32[64,256]{1,0:T(8,128)S(1)}, f32[64,256]{1,0:T(8,128)S(1)}, u32[]{:S(2)}, u32[]{:S(2)}) collective-permute-start(f32[64,256]{1,0:T(8,128)S(1)} %get-tuple-element.51.refs_0_), channel_id=1, source_target_pairs={{0,2},{1,3},{2,0},{3,1},{4,6},{5,7},{6,4},{7,5},{8,10},{9,11},{10,... | collective-permute-start | bytes 196616 | tf_op jit(solution)/shard_map/ppermute | solution.py:33
  27.1 11.8 %collective-permute-start.8 = (f32[64,256]{1,0:T(8,128)S(1)}, f32[64,256]{1,0:T(8,128)S(1)}, u32[]{:S(2)}, u32[]{:S(2)}) collective-permute-start(f32[64,256]{1,0:T(8,128)S(1)} %get-tuple-element.51.refs_0_), channel_id=1, source_target_pairs={{0,3},{1,2},{2,1},{3,0},{4,7},{5,6},{6,5},{7,4},{8,11},{9,10},{10,... | collective-permute-start | bytes 196616 | tf_op jit(solution)/shard_map/ppermute | solution.py:33
  28.4 8.4 %collective-permute-start.13 = (f32[64,256]{1,0:T(8,128)S(1)}, f32[64,256]{1,0:T(8,128)S(1)}, u32[]{:S(2)}, u32[]{:S(2)}) collective-permute-start(f32[64,256]{1,0:T(8,128)S(1)} %get-tuple-element.55.refs_1_), channel_id=1, source_target_pairs={{0,2},{1,3},{2,0},{3,1},{4,6},{5,7},{6,4},{7,5},{8,10},{9,11},{10,... | collective-permute-start | bytes 196616 | tf_op jit(solution)/shard_map/ppermute | solution.py:33
  30.5 6.4 %collective-permute-start.14 = (f32[64,256]{1,0:T(8,128)S(1)}, f32[64,256]{1,0:T(8,128)S(1)}, u32[]{:S(2)}, u32[]{:S(2)}) collective-permute-start(f32[64,256]{1,0:T(8,128)S(1)} %get-tuple-element.55.refs_1_), channel_id=1, source_target_pairs={{0,3},{1,2},{2,1},{3,0},{4,7},{5,6},{6,5},{7,4},{8,11},{9,10},{10,... | collective-permute-start | bytes 196616 | tf_op jit(solution)/shard_map/ppermute | solution.py:33
  37.5 6.7 %collective-permute-start.15 = (f32[64,256]{1,0:T(8,128)S(1)}, f32[64,256]{1,0:T(8,128)S(1)}, u32[]{:S(2)}, u32[]{:S(2)}) collective-permute-start(f32[64,256]{1,0:T(8,128)S(1)} %get-tuple-element.57), channel_id=1, source_target_pairs={{0,1},{1,0},{2,3},{3,2},{4,5},{5,4},{6,7},{7,6},{8,9},{9,8},{10,11... | collective-permute-start | bytes 196616 | tf_op jit(solution)/shard_map/ppermute | solution.py:33
  39.6 14.0 %collective-permute-start.9 = (f32[64,256]{1,0:T(8,128)S(1)}, f32[64,256]{1,0:T(8,128)S(1)}, u32[]{:S(2)}, u32[]{:S(2)}) collective-permute-start(f32[64,256]{1,0:T(8,128)S(1)} %get-tuple-element.53), channel_id=1, source_target_pairs={{0,1},{1,0},{2,3},{3,2},{4,5},{5,4},{6,7},{7,6},{8,9},{9,8},{10,11... | collective-permute-start | bytes 196616 | tf_op jit(solution)/shard_map/ppermute | solution.py:33
  40.4 13.1 %collective-permute-start.10 = (f32[64,256]{1,0:T(8,128)S(1)}, f32[64,256]{1,0:T(8,128)S(1)}, u32[]{:S(2)}, u32[]{:S(2)}) collective-permute-start(f32[64,256]{1,0:T(8,128)S(1)} %get-tuple-element.53), channel_id=1, source_target_pairs={{0,2},{1,3},{2,0},{3,1},{4,6},{5,7},{6,4},{7,5},{8,10},{9,11},{10,... | collective-permute-start | bytes 196616 | tf_op jit(solution)/shard_map/ppermute | solution.py:33
  41.9 11.7 %collective-permute-start.11 = (f32[64,256]{1,0:T(8,128)S(1)}, f32[64,256]{1,0:T(8,128)S(1)}, u32[]{:S(2)}, u32[]{:S(2)}) collective-permute-start(f32[64,256]{1,0:T(8,128)S(1)} %get-tuple-element.53), channel_id=1, source_target_pairs={{0,3},{1,2},{2,1},{3,0},{4,7},{5,6},{6,5},{7,4},{8,11},{9,10},{10,... | collective-permute-start | bytes 196616 | tf_op jit(solution)/shard_map/ppermute | solution.py:33
  44.0 7.5 %collective-permute-start.16 = (f32[64,256]{1,0:T(8,128)S(1)}, f32[64,256]{1,0:T(8,128)S(1)}, u32[]{:S(2)}, u32[]{:S(2)}) collective-permute-start(f32[64,256]{1,0:T(8,128)S(1)} %get-tuple-element.57), channel_id=1, source_target_pairs={{0,2},{1,3},{2,0},{3,1},{4,6},{5,7},{6,4},{7,5},{8,10},{9,11},{10,... | collective-permute-start | bytes 196616 | tf_op jit(solution)/shard_map/ppermute | solution.py:33
  44.3 7.3 %collective-permute-start.17 = (f32[64,256]{1,0:T(8,128)S(1)}, f32[64,256]{1,0:T(8,128)S(1)}, u32[]{:S(2)}, u32[]{:S(2)}) collective-permute-start(f32[64,256]{1,0:T(8,128)S(1)} %get-tuple-element.57), channel_id=1, source_target_pairs={{0,3},{1,2},{2,1},{3,0},{4,7},{5,6},{6,5},{7,4},{8,11},{9,10},{10,... | collective-permute-start | bytes 196616 | tf_op jit(solution)/shard_map/ppermute | solution.py:33
  52.2 6.7 %collective-permute-start.24 = (f32[64,256]{1,0:T(8,128)S(1)}, f32[64,256]{1,0:T(8,128)S(1)}, u32[]{:S(2)}, u32[]{:S(2)}) collective-permute-start(f32[64,256]{1,0:T(8,128)S(1)} %get-tuple-element.63.refs_3_), channel_id=1, source_target_pairs={{0,1},{1,0},{2,3},{3,2},{4,5},{5,4},{6,7},{7,6},{8,9},{9,8},{10,11... | collective-permute-start | bytes 196616 | tf_op jit(solution)/shard_map/ppermute | solution.py:33
  54.2 13.9 %collective-permute-start.18 = (f32[64,256]{1,0:T(8,128)S(1)}, f32[64,256]{1,0:T(8,128)S(1)}, u32[]{:S(2)}, u32[]{:S(2)}) collective-permute-start(f32[64,256]{1,0:T(8,128)S(1)} %get-tuple-element.59.refs_2_), channel_id=1, source_target_pairs={{0,1},{1,0},{2,3},{3,2},{4,5},{5,4},{6,7},{7,6},{8,9},{9,8},{10,11... | collective-permute-start | bytes 196616 | tf_op jit(solution)/shard_map/ppermute | solution.py:33
  55.1 13.1 %collective-permute-start.19 = (f32[64,256]{1,0:T(8,128)S(1)}, f32[64,256]{1,0:T(8,128)S(1)}, u32[]{:S(2)}, u32[]{:S(2)}) collective-permute-start(f32[64,256]{1,0:T(8,128)S(1)} %get-tuple-element.59.refs_2_), channel_id=1, source_target_pairs={{0,2},{1,3},{2,0},{3,1},{4,6},{5,7},{6,4},{7,5},{8,10},{9,11},{10,... | collective-permute-start | bytes 196616 | tf_op jit(solution)/shard_map/ppermute | solution.py:33
  56.7 11.6 %collective-permute-start.20 = (f32[64,256]{1,0:T(8,128)S(1)}, f32[64,256]{1,0:T(8,128)S(1)}, u32[]{:S(2)}, u32[]{:S(2)}) collective-permute-start(f32[64,256]{1,0:T(8,128)S(1)} %get-tuple-element.59.refs_2_), channel_id=1, source_target_pairs={{0,3},{1,2},{2,1},{3,0},{4,7},{5,6},{6,5},{7,4},{8,11},{9,10},{10,... | collective-permute-start | bytes 196616 | tf_op jit(solution)/shard_map/ppermute | solution.py:33
  58.7 7.5 %collective-permute-start.25 = (f32[64,256]{1,0:T(8,128)S(1)}, f32[64,256]{1,0:T(8,128)S(1)}, u32[]{:S(2)}, u32[]{:S(2)}) collective-permute-start(f32[64,256]{1,0:T(8,128)S(1)} %get-tuple-element.63.refs_3_), channel_id=1, source_target_pairs={{0,2},{1,3},{2,0},{3,1},{4,6},{5,7},{6,4},{7,5},{8,10},{9,11},{10,... | collective-permute-start | bytes 196616 | tf_op jit(solution)/shard_map/ppermute | solution.py:33
  59.0 7.2 %collective-permute-start.26 = (f32[64,256]{1,0:T(8,128)S(1)}, f32[64,256]{1,0:T(8,128)S(1)}, u32[]{:S(2)}, u32[]{:S(2)}) collective-permute-start(f32[64,256]{1,0:T(8,128)S(1)} %get-tuple-element.63.refs_3_), channel_id=1, source_target_pairs={{0,3},{1,2},{2,1},{3,0},{4,7},{5,6},{6,5},{7,4},{8,11},{9,10},{10,... | collective-permute-start | bytes 196616 | tf_op jit(solution)/shard_map/ppermute | solution.py:33
  66.9 7.0 %collective-permute-start.27 = (f32[64,256]{1,0:T(8,128)S(1)}, f32[64,256]{1,0:T(8,128)S(1)}, u32[]{:S(2)}, u32[]{:S(2)}) collective-permute-start(f32[64,256]{1,0:T(8,128)S(1)} %get-tuple-element.65), channel_id=1, source_target_pairs={{0,1},{1,0},{2,3},{3,2},{4,5},{5,4},{6,7},{7,6},{8,9},{9,8},{10,11... | collective-permute-start | bytes 196616 | tf_op jit(solution)/shard_map/ppermute | solution.py:33
  68.9 15.4 %collective-permute-start.21 = (f32[64,256]{1,0:T(8,128)S(1)}, f32[64,256]{1,0:T(8,128)S(1)}, u32[]{:S(2)}, u32[]{:S(2)}) collective-permute-start(f32[64,256]{1,0:T(8,128)S(1)} %get-tuple-element.61), channel_id=1, source_target_pairs={{0,1},{1,0},{2,3},{3,2},{4,5},{5,4},{6,7},{7,6},{8,9},{9,8},{10,11... | collective-permute-start | bytes 196616 | tf_op jit(solution)/shard_map/ppermute | solution.py:33
  69.8 16.4 %collective-permute-start.22 = (f32[64,256]{1,0:T(8,128)S(1)}, f32[64,256]{1,0:T(8,128)S(1)}, u32[]{:S(2)}, u32[]{:S(2)}) collective-permute-start(f32[64,256]{1,0:T(8,128)S(1)} %get-tuple-element.61), channel_id=1, source_target_pairs={{0,2},{1,3},{2,0},{3,1},{4,6},{5,7},{6,4},{7,5},{8,10},{9,11},{10,... | collective-permute-start | bytes 196616 | tf_op jit(solution)/shard_map/ppermute | solution.py:33
  71.6 14.6 %collective-permute-start.23 = (f32[64,256]{1,0:T(8,128)S(1)}, f32[64,256]{1,0:T(8,128)S(1)}, u32[]{:S(2)}, u32[]{:S(2)}) collective-permute-start(f32[64,256]{1,0:T(8,128)S(1)} %get-tuple-element.61), channel_id=1, source_target_pairs={{0,3},{1,2},{2,1},{3,0},{4,7},{5,6},{6,5},{7,4},{8,11},{9,10},{10,... | collective-permute-start | bytes 196616 | tf_op jit(solution)/shard_map/ppermute | solution.py:33
  73.4 7.7 %collective-permute-start.28 = (f32[64,256]{1,0:T(8,128)S(1)}, f32[64,256]{1,0:T(8,128)S(1)}, u32[]{:S(2)}, u32[]{:S(2)}) collective-permute-start(f32[64,256]{1,0:T(8,128)S(1)} %get-tuple-element.65), channel_id=1, source_target_pairs={{0,2},{1,3},{2,0},{3,1},{4,6},{5,7},{6,4},{7,5},{8,10},{9,11},{10,... | collective-permute-start | bytes 196616 | tf_op jit(solution)/shard_map/ppermute | solution.py:33
  73.9 7.2 %collective-permute-start.29 = (f32[64,256]{1,0:T(8,128)S(1)}, f32[64,256]{1,0:T(8,128)S(1)}, u32[]{:S(2)}, u32[]{:S(2)}) collective-permute-start(f32[64,256]{1,0:T(8,128)S(1)} %get-tuple-element.65), channel_id=1, source_target_pairs={{0,3},{1,2},{2,1},{3,0},{4,7},{5,6},{6,5},{7,4},{8,11},{9,10},{10,... | collective-permute-start | bytes 196616 | tf_op jit(solution)/shard_map/ppermute | solution.py:33
  81.7 7.8 %collective-permute-start.36 = (f32[64,256]{1,0:T(8,128)S(1)}, f32[64,256]{1,0:T(8,128)S(1)}, u32[]{:S(2)}, u32[]{:S(2)}) collective-permute-start(f32[64,256]{1,0:T(8,128)S(1)} %get-tuple-element.71.refs_5_), channel_id=1, source_target_pairs={{0,1},{1,0},{2,3},{3,2},{4,5},{5,4},{6,7},{7,6},{8,9},{9,8},{10,11... | collective-permute-start | bytes 196616 | tf_op jit(solution)/shard_map/ppermute | solution.py:33
  83.0 8.7 %collective-permute-start.37 = (f32[64,256]{1,0:T(8,128)S(1)}, f32[64,256]{1,0:T(8,128)S(1)}, u32[]{:S(2)}, u32[]{:S(2)}) collective-permute-start(f32[64,256]{1,0:T(8,128)S(1)} %get-tuple-element.71.refs_5_), channel_id=1, source_target_pairs={{0,2},{1,3},{2,0},{3,1},{4,6},{5,7},{6,4},{7,5},{8,10},{9,11},{10,... | collective-permute-start | bytes 196616 | tf_op jit(solution)/shard_map/ppermute | solution.py:33
  84.4 7.4 %collective-permute-start.38 = (f32[64,256]{1,0:T(8,128)S(1)}, f32[64,256]{1,0:T(8,128)S(1)}, u32[]{:S(2)}, u32[]{:S(2)}) collective-permute-start(f32[64,256]{1,0:T(8,128)S(1)} %get-tuple-element.71.refs_5_), channel_id=1, source_target_pairs={{0,3},{1,2},{2,1},{3,0},{4,7},{5,6},{6,5},{7,4},{8,11},{9,10},{10,... | collective-permute-start | bytes 196616 | tf_op jit(solution)/shard_map/ppermute | solution.py:33
  86.9 10.9 %collective-permute-start.30 = (f32[64,256]{1,0:T(8,128)S(1)}, f32[64,256]{1,0:T(8,128)S(1)}, u32[]{:S(2)}, u32[]{:S(2)}) collective-permute-start(f32[64,256]{1,0:T(8,128)S(1)} %get-tuple-element.67.refs_4_), channel_id=1, source_target_pairs={{0,1},{1,0},{2,3},{3,2},{4,5},{5,4},{6,7},{7,6},{8,9},{9,8},{10,11... | collective-permute-start | bytes 196616 | tf_op jit(solution)/shard_map/ppermute | solution.py:33
  87.3 12.4 %collective-permute-start.31 = (f32[64,256]{1,0:T(8,128)S(1)}, f32[64,256]{1,0:T(8,128)S(1)}, u32[]{:S(2)}, u32[]{:S(2)}) collective-permute-start(f32[64,256]{1,0:T(8,128)S(1)} %get-tuple-element.67.refs_4_), channel_id=1, source_target_pairs={{0,2},{1,3},{2,0},{3,1},{4,6},{5,7},{6,4},{7,5},{8,10},{9,11},{10,... | collective-permute-start | bytes 196616 | tf_op jit(solution)/shard_map/ppermute | solution.py:33
  89.5 10.2 %collective-permute-start.32 = (f32[64,256]{1,0:T(8,128)S(1)}, f32[64,256]{1,0:T(8,128)S(1)}, u32[]{:S(2)}, u32[]{:S(2)}) collective-permute-start(f32[64,256]{1,0:T(8,128)S(1)} %get-tuple-element.67.refs_4_), channel_id=1, source_target_pairs={{0,3},{1,2},{2,1},{3,0},{4,7},{5,6},{6,5},{7,4},{8,11},{9,10},{10,... | collective-permute-start | bytes 196616 | tf_op jit(solution)/shard_map/ppermute | solution.py:33
  91.8 28.2 %copy-start = (f32[1,1,3,128,1024]{4,3,2,1,0:T(8,128)S(1)}, f32[1,1,3,128,1024]{4,3,2,1,0:T(8,128)}, u32[]{:S(2)}) copy-start(f32[1,1,3,128,1024]{4,3,2,1,0:T(8,128)} %param.13) | copy-start | bytes 4718596
  91.8 28.2 %copy-start.5 = (s32[1,1,3]{2,1,0:T(1,128)S(1)}, s32[1,1,3]{2,1,0:T(1,128)}, u32[]{:S(2)}) copy-start(s32[1,1,3]{2,1,0:T(1,128)} %refs_6_.1) | copy-start | bytes 40
  92.4 10.6 %collective-permute-start.39 = (f32[64,256]{1,0:T(8,128)S(1)}, f32[64,256]{1,0:T(8,128)S(1)}, u32[]{:S(2)}, u32[]{:S(2)}) collective-permute-start(f32[64,256]{1,0:T(8,128)S(1)} %get-tuple-element.73), channel_id=1, source_target_pairs={{0,1},{1,0},{2,3},{3,2},{4,5},{5,4},{6,7},{7,6},{8,9},{9,8},{10,11... | collective-permute-start | bytes 196616 | tf_op jit(solution)/shard_map/ppermute | solution.py:33
  97.2 7.7 %collective-permute-start.40 = (f32[64,256]{1,0:T(8,128)S(1)}, f32[64,256]{1,0:T(8,128)S(1)}, u32[]{:S(2)}, u32[]{:S(2)}) collective-permute-start(f32[64,256]{1,0:T(8,128)S(1)} %get-tuple-element.73), channel_id=1, source_target_pairs={{0,2},{1,3},{2,0},{3,1},{4,6},{5,7},{6,4},{7,5},{8,10},{9,11},{10,... | collective-permute-start | bytes 196616 | tf_op jit(solution)/shard_map/ppermute | solution.py:33
  97.8 10.4 %collective-permute-start.41 = (f32[64,256]{1,0:T(8,128)S(1)}, f32[64,256]{1,0:T(8,128)S(1)}, u32[]{:S(2)}, u32[]{:S(2)}) collective-permute-start(f32[64,256]{1,0:T(8,128)S(1)} %get-tuple-element.73), channel_id=1, source_target_pairs={{0,3},{1,2},{2,1},{3,0},{4,7},{5,6},{6,5},{7,4},{8,11},{9,10},{10,... | collective-permute-start | bytes 196616 | tf_op jit(solution)/shard_map/ppermute | solution.py:33
  100.4 4.5 %collective-permute-start.33 = (f32[64,256]{1,0:T(8,128)S(1)}, f32[64,256]{1,0:T(8,128)S(1)}, u32[]{:S(2)}, u32[]{:S(2)}) collective-permute-start(f32[64,256]{1,0:T(8,128)S(1)} %get-tuple-element.69), channel_id=1, source_target_pairs={{0,1},{1,0},{2,3},{3,2},{4,5},{5,4},{6,7},{7,6},{8,9},{9,8},{10,11... | collective-permute-start | bytes 196616 | tf_op jit(solution)/shard_map/ppermute | solution.py:33
  101.5 6.7 %collective-permute-start.34 = (f32[64,256]{1,0:T(8,128)S(1)}, f32[64,256]{1,0:T(8,128)S(1)}, u32[]{:S(2)}, u32[]{:S(2)}) collective-permute-start(f32[64,256]{1,0:T(8,128)S(1)} %get-tuple-element.69), channel_id=1, source_target_pairs={{0,2},{1,3},{2,0},{3,1},{4,6},{5,7},{6,4},{7,5},{8,10},{9,11},{10,... | collective-permute-start | bytes 196616 | tf_op jit(solution)/shard_map/ppermute | solution.py:33
  103.0 6.2 %collective-permute-start.35 = (f32[64,256]{1,0:T(8,128)S(1)}, f32[64,256]{1,0:T(8,128)S(1)}, u32[]{:S(2)}, u32[]{:S(2)}) collective-permute-start(f32[64,256]{1,0:T(8,128)S(1)} %get-tuple-element.69), channel_id=1, source_target_pairs={{0,3},{1,2},{2,1},{3,0},{4,7},{5,6},{6,5},{7,4},{8,11},{9,10},{10,... | collective-permute-start | bytes 196616 | tf_op jit(solution)/shard_map/ppermute | solution.py:33
  109.9 8.5 %collective-permute-start.42 = (f32[64,256]{1,0:T(8,128)S(1)}, f32[64,256]{1,0:T(8,128)S(1)}, u32[]{:S(2)}, u32[]{:S(2)}) collective-permute-start(f32[64,256]{1,0:T(8,128)S(1)} %get-tuple-element.75.refs_6_), channel_id=1, source_target_pairs={{0,1},{1,0},{2,3},{3,2},{4,5},{5,4},{6,7},{7,6},{8,9},{9,8},{10,11... | collective-permute-start | bytes 196616 | tf_op jit(solution)/shard_map/ppermute | solution.py:33
  112.4 7.6 %collective-permute-start.43 = (f32[64,256]{1,0:T(8,128)S(1)}, f32[64,256]{1,0:T(8,128)S(1)}, u32[]{:S(2)}, u32[]{:S(2)}) collective-permute-start(f32[64,256]{1,0:T(8,128)S(1)} %get-tuple-element.75.refs_6_), channel_id=1, source_target_pairs={{0,2},{1,3},{2,0},{3,1},{4,6},{5,7},{6,4},{7,5},{8,10},{9,11},{10,... | collective-permute-start | bytes 196616 | tf_op jit(solution)/shard_map/ppermute | solution.py:33
  113.3 6.7 %collective-permute-start.44 = (f32[64,256]{1,0:T(8,128)S(1)}, f32[64,256]{1,0:T(8,128)S(1)}, u32[]{:S(2)}, u32[]{:S(2)}) collective-permute-start(f32[64,256]{1,0:T(8,128)S(1)} %get-tuple-element.75.refs_6_), channel_id=1, source_target_pairs={{0,3},{1,2},{2,1},{3,0},{4,7},{5,6},{6,5},{7,4},{8,11},{9,10},{10,... | collective-permute-start | bytes 196616 | tf_op jit(solution)/shard_map/ppermute | solution.py:33
  115.5 6.1 %collective-permute-start.45 = (f32[64,256]{1,0:T(8,128)S(1)}, f32[64,256]{1,0:T(8,128)S(1)}, u32[]{:S(2)}, u32[]{:S(2)}) collective-permute-start(f32[64,256]{1,0:T(8,128)S(1)} %get-tuple-element.77.refs_7_), channel_id=1, source_target_pairs={{0,1},{1,0},{2,3},{3,2},{4,5},{5,4},{6,7},{7,6},{8,9},{9,8},{10,11... | collective-permute-start | bytes 196616 | tf_op jit(solution)/shard_map/ppermute | solution.py:33
  116.6 5.9 %collective-permute-start.46 = (f32[64,256]{1,0:T(8,128)S(1)}, f32[64,256]{1,0:T(8,128)S(1)}, u32[]{:S(2)}, u32[]{:S(2)}) collective-permute-start(f32[64,256]{1,0:T(8,128)S(1)} %get-tuple-element.77.refs_7_), channel_id=1, source_target_pairs={{0,2},{1,3},{2,0},{3,1},{4,6},{5,7},{6,4},{7,5},{8,10},{9,11},{10,... | collective-permute-start | bytes 196616 | tf_op jit(solution)/shard_map/ppermute | solution.py:33
  118.4 6.1 %collective-permute-start.47 = (f32[64,256]{1,0:T(8,128)S(1)}, f32[64,256]{1,0:T(8,128)S(1)}, u32[]{:S(2)}, u32[]{:S(2)}) collective-permute-start(f32[64,256]{1,0:T(8,128)S(1)} %get-tuple-element.77.refs_7_), channel_id=1, source_target_pairs={{0,3},{1,2},{2,1},{3,0},{4,7},{5,6},{6,5},{7,4},{8,11},{9,10},{10,... | collective-permute-start | bytes 196616 | tf_op jit(solution)/shard_map/ppermute | solution.py:33
  126.2 1.4 collective-permute-start.48
  127.6 4.6 %collective-permute-start.49 = (f32[2,16,512]{2,1,0:T(8,128)S(1)}, f32[2,16,512]{2,1,0:T(8,128)S(1)}, u32[]{:S(2)}, u32[]{:S(2)}) collective-permute-start(f32[2,16,512]{2,1,0:T(8,128)S(1)} %get-tuple-element.37), channel_id=1, source_target_pairs={{0,8},{4,12},{8,0},{12,4},{16,24},{20,28},{24,16},{28,20},{1,9},{5... | collective-permute-start | bytes 196616 | tf_op jit(solution)/shard_map/ppermute | solution.py:61
  129.2 4.3 %collective-permute-start.50 = (f32[2,16,512]{2,1,0:T(8,128)S(1)}, f32[2,16,512]{2,1,0:T(8,128)S(1)}, u32[]{:S(2)}, u32[]{:S(2)}) collective-permute-start(f32[2,16,512]{2,1,0:T(8,128)S(1)} %get-tuple-element.38), channel_id=1, source_target_pairs={{0,16},{4,20},{8,24},{12,28},{16,0},{20,4},{24,8},{28,12},{1,17},{... | collective-permute-start | bytes 196616 | tf_op jit(solution)/shard_map/ppermute | solution.py:61
  130.7 5.2 %collective-permute-start.51 = (f32[2,16,512]{2,1,0:T(8,128)S(1)}, f32[2,16,512]{2,1,0:T(8,128)S(1)}, u32[]{:S(2)}, u32[]{:S(2)}) collective-permute-start(f32[2,16,512]{2,1,0:T(8,128)S(1)} %get-tuple-element.39), channel_id=1, source_target_pairs={{0,24},{4,28},{8,16},{12,20},{16,8},{20,12},{24,0},{28,4},{1,25},{... | collective-permute-start | bytes 196616 | tf_op jit(solution)/shard_map/ppermute | solution.py:61
  137.3 4.9 %collective-permute-start.52 = (f32[16,1280]{1,0:T(8,128)S(1)}, f32[16,1280]{1,0:T(8,128)S(1)}, u32[]{:S(2)}, u32[]{:S(2)}) collective-permute-start(f32[16,1280]{1,0:T(8,128)S(1)} %get-tuple-element.41), channel_id=1, source_target_pairs={{0,1},{1,0},{2,3},{3,2},{4,5},{5,4},{6,7},{7,6},{8,9},{9,8},{10,11... | collective-permute-start | bytes 245768 | tf_op jit(solution)/shard_map/ppermute | solution.py:33
  137.4 7.3 %collective-permute-start.53 = (f32[16,1280]{1,0:T(8,128)S(1)}, f32[16,1280]{1,0:T(8,128)S(1)}, u32[]{:S(2)}, u32[]{:S(2)}) collective-permute-start(f32[16,1280]{1,0:T(8,128)S(1)} %get-tuple-element.42), channel_id=1, source_target_pairs={{0,2},{1,3},{2,0},{3,1},{4,6},{5,7},{6,4},{7,5},{8,10},{9,11},{10,... | collective-permute-start | bytes 245768 | tf_op jit(solution)/shard_map/ppermute | solution.py:33
  139.6 6.3 %collective-permute-start.54 = (f32[16,1280]{1,0:T(8,128)S(1)}, f32[16,1280]{1,0:T(8,128)S(1)}, u32[]{:S(2)}, u32[]{:S(2)}) collective-permute-start(f32[16,1280]{1,0:T(8,128)S(1)} %get-tuple-element.43), channel_id=1, source_target_pairs={{0,3},{1,2},{2,1},{3,0},{4,7},{5,6},{6,5},{7,4},{8,11},{9,10},{10,... | collective-permute-start | bytes 245768 | tf_op jit(solution)/shard_map/ppermute | solution.py:33
  146.4 4.4 %collective-permute-start.55 = (f32[16,256]{1,0:T(8,128)S(1)}, f32[16,256]{1,0:T(8,128)S(1)}, u32[]{:S(2)}, u32[]{:S(2)}) collective-permute-start(f32[16,256]{1,0:T(8,128)S(1)} %get-tuple-element.46.refs_0_), channel_id=1, source_target_pairs={{0,1},{1,0},{2,3},{3,2},{4,5},{5,4},{6,7},{7,6},{8,9},{9,8},{10,11... | collective-permute-start | bytes 49160 | tf_op jit(solution)/shard_map/ppermute | solution.py:33
  147.5 4.6 %collective-permute-start.56 = (f32[16,256]{1,0:T(8,128)S(1)}, f32[16,256]{1,0:T(8,128)S(1)}, u32[]{:S(2)}, u32[]{:S(2)}) collective-permute-start(f32[16,256]{1,0:T(8,128)S(1)} %get-tuple-element.46.refs_0_), channel_id=1, source_target_pairs={{0,2},{1,3},{2,0},{3,1},{4,6},{5,7},{6,4},{7,5},{8,10},{9,11},{10,... | collective-permute-start | bytes 49160 | tf_op jit(solution)/shard_map/ppermute | solution.py:33
  149.2 5.6 %collective-permute-start.57 = (f32[16,256]{1,0:T(8,128)S(1)}, f32[16,256]{1,0:T(8,128)S(1)}, u32[]{:S(2)}, u32[]{:S(2)}) collective-permute-start(f32[16,256]{1,0:T(8,128)S(1)} %get-tuple-element.46.refs_0_), channel_id=1, source_target_pairs={{0,3},{1,2},{2,1},{3,0},{4,7},{5,6},{6,5},{7,4},{8,11},{9,10},{10,... | collective-permute-start | bytes 49160 | tf_op jit(solution)/shard_map/ppermute | solution.py:33
  155.3 4.4 %collective-permute-start.58 = (f32[16,256]{1,0:T(8,128)S(1)}, f32[16,256]{1,0:T(8,128)S(1)}, u32[]{:S(2)}, u32[]{:S(2)}) collective-permute-start(f32[16,256]{1,0:T(8,128)S(1)} %shard_map.122.refs_0_), channel_id=1, source_target_pairs={{0,1},{1,0},{2,3},{3,2},{4,5},{5,4},{6,7},{7,6},{8,9},{9,8},{10,11... | collective-permute-start | bytes 49160 | tf_op jit(solution)/shard_map/ppermute | solution.py:33
  155.3 4.7 %collective-permute-start.59 = (f32[16,256]{1,0:T(8,128)S(1)}, f32[16,256]{1,0:T(8,128)S(1)}, u32[]{:S(2)}, u32[]{:S(2)}) collective-permute-start(f32[16,256]{1,0:T(8,128)S(1)} %shard_map.122.refs_0_), channel_id=1, source_target_pairs={{0,2},{1,3},{2,0},{3,1},{4,6},{5,7},{6,4},{7,5},{8,10},{9,11},{10,... | collective-permute-start | bytes 49160 | tf_op jit(solution)/shard_map/ppermute | solution.py:33
  157.5 5.5 %collective-permute-start.60 = (f32[16,256]{1,0:T(8,128)S(1)}, f32[16,256]{1,0:T(8,128)S(1)}, u32[]{:S(2)}, u32[]{:S(2)}) collective-permute-start(f32[16,256]{1,0:T(8,128)S(1)} %shard_map.122.refs_0_), channel_id=1, source_target_pairs={{0,3},{1,2},{2,1},{3,0},{4,7},{5,6},{6,5},{7,4},{8,11},{9,10},{10,... | collective-permute-start | bytes 49160 | tf_op jit(solution)/shard_map/ppermute | solution.py:33
  (6 other events, 112.3 us)

commit v10 on v9

--- a/solution.py
+++ b/solution.py
@@ -49,6 +49,16 @@
     for offset, piece in pieces:
         whole = lax.dynamic_update_slice_in_dim(whole, piece, offset, 1)
     return whole
+
+
+def apply_pieces(factor, index, pieces):
+    total = None
+    for offset, piece in pieces:
+        size = (1, 1, factor.shape[2], piece.shape[1])
+        columns = lax.dynamic_slice(factor, (0, index, 0, offset), size)[0, 0]
+        term = contract_last(piece, columns)
+        total = term if total is None else total + term
+    return total
 
 
 def swap(value, axis, distance, block):
@@ -386,14 +396,19 @@
     for current in range(supernodes):
         owned = []
         for residual in residuals:
-            whole = assemble(gather_rows(residual), order)
-            owned.append(contract_last(whole, diag_inv_local[0, current]))
+            pieces = gather_rows(residual)
+            if current:
+                owned.append(apply_pieces(diag_inv_local, current, pieces))
+            else:
+                whole = assemble(pieces, order)
+                owned.append(contract_last(whole, diag_inv_local[0, current]))
         solved.append(owned)
-        gathered.append([assemble(gather_rows(value), order) for value in owned])
+        held = [gather_rows(value) for value in owned]
+        gathered.append([assemble(pieces, order) for pieces in held])
         if current + 1 < supernodes:
             residuals = [
-                later[current * streams + i] - contract_last(whole, sub_local[0, current])
-                for i, whole in enumerate(gathered[-1])
+                later[current * streams + i] - apply_pieces(sub_local, current, pieces)
+                for i, pieces in enumerate(held)
             ]
 
     by_stream = [[values[i] for values in gathered] for i in range(streams)]

time: 164 us -> 154 us (0.939)
  waiting for transfers between devices: 47.8 us -> 30.9 us
  matrix products: 11.4 us -> 17.3 us
  local copies, waits for them, and re-layouts: 3.83 us -> 9.14 us
  starting transfers between devices: 91.5 us -> 86.2 us
    ppermute x57, waiting for transfers between devices: 42.8 us -> 25.8 us  [send(): return lax.ppermute(value, axis, pairs)]
    dot_general x14 -> x50, matrix products: 11.4 us -> 17.3 us  [contract_last(): lax.dot_general(left, right, (((left.ndim - 1,), (right.ndim - 1,)), ((),...]
    ppermute x57, starting transfers between devices: 87.9 us -> 82.6 us  [send(): return lax.ppermute(value, axis, pairs)]
    dynamic_update_slice x49 -> x32, local copies, waits for them, and re-layouts: 0.5 us -> 4.53 us  [assemble(): whole = lax.dynamic_update_slice_in_dim(whole, piece, offset, 1)]
  transfers between devices with their start and end apart: 61 -> 61, of which waited for: 20 -> 19; matrix products, arithmetic and copies ran while one was open for 8% -> 15% of each run, Pallas kernels for 2% -> 2%
where the time goes in v10:
time: 154 us; the launch traced here: 153 us
  starting transfers between devices  86.2 us (56%)
  waiting for transfers between devices  30.9 us (20%)
  matrix products  17.3 us (11%)
  local copies, waits for them, and re-layouts  9.14 us (6%)
  Pallas kernels  6.79 us (4%)
  between operations  2.36 us (2%)
    ppermute x57, starting transfers between devices, send(): return lax.ppermute(value, axis, pairs)  82.6 us
    ppermute x57, waiting for transfers between devices, send(): return lax.ppermute(value, axis, pairs)  25.8 us
    dot_general x50, matrix products, contract_last(): lax.dot_general(left, right, (((left.ndim - 1,), (right.ndim - 1,)), ((),...  17.3 us
    pallas_call x11, Pallas kernels, local_kernel(): pl.pallas_call(body, out_shape=list(outs), in_specs=specs or [VMEM] * len...  6.79 us
    dynamic_update_slice x32, local copies, waits for them, and re-layouts, assemble(): whole = lax.dynamic_update_slice_in_dim(whole, piece, offset, 1)  4.53 us
    ppermute x3, waiting for transfers between devices, swap(): return lax.ppermute(value, axis, pairs)  3.69 us
    ppermute x3, starting transfers between devices, swap(): return lax.ppermute(value, axis, pairs)  3.55 us
  transfers between devices with their start and end apart: 61, of which 19 were waited for; matrix products, arithmetic and copies ran while one was open for 15% of the time, Pallas kernels for 2%

profile of v10, /device:TPU:0, one launch (start us, length us, event | category | flops | bytes accessed | tf_op | source)
XLA Modules:
  0.0 153.3 jit_solution(11275639257119422299)
XLA Ops:
  0.6 1.1 slice.10.rhs_ref
  1.8 5.1 %collective-permute-start.2 = (f32[64,256]{1,0:T(8,128)S(1)}, f32[64,256]{1,0:T(8,128)}, u32[]{:S(2)}, u32[]{:S(2)}) collective-permute-start(f32[64,256]{1,0:T(8,128)S(1)} %get-tuple-element.26), channel_id=1, source_target_pairs={{0,3},{1,2},{2,1},{3,0},{4,7},{5,6},{6,5},{7,4},{8,11},{9,10},{10,... | collective-permute-start | bytes 196616 | tf_op jit(solution)/shard_map/ppermute | solution.py:33
  7.6 3.7 %collective-permute-start.5 = (f32[64,256]{1,0:T(8,128)S(1)}, f32[64,256]{1,0:T(8,128)}, u32[]{:S(2)}, u32[]{:S(2)}) collective-permute-start(f32[64,256]{1,0:T(8,128)S(1)} %get-tuple-element.27), channel_id=1, source_target_pairs={{0,3},{1,2},{2,1},{3,0},{4,7},{5,6},{6,5},{7,4},{8,11},{9,10},{10,... | collective-permute-start | bytes 196616 | tf_op jit(solution)/shard_map/ppermute | solution.py:33
  11.3 1.0 slice.12.rhs_ref
  14.5 1.2 collective-permute-done.3
  16.9 4.7 %collective-permute-done.4 = f32[64,256]{1,0:T(8,128)S(1)} collective-permute-done((f32[64,256]{1,0:T(8,128)S(1)}, f32[64,256]{1,0:T(8,128)S(1)}, u32[]{:S(2)}, u32[]{:S(2)}) %collective-permute-start.4) | collective-permute-done | bytes 65568 | tf_op jit(solution)/shard_map/ppermute | solution.py:33
  21.6 0.9 constant_dynamic-update-slice_fusion.32
  22.5 1.8 %constant_dynamic-update-slice_fusion.15 = (f32[64,1024]{1,0:T(8,128)S(1)}, f32[64,256]{1,0:T(8,128)S(1)}) fusion(f32[64,1024]{1,0:T(8,128)S(1)} %broadcast.3.clone.2, s32[]{:T(128)S(6)} %select_n.8, f32[64,1024]{1,0:T(8,128)S(1)} %constant_dynamic-update-slice_fusion.32, f32[1,4,256,1024]{3,2,1,0:T(8,128)} %param.11), kind=kOutput, calls=%fused_computation.208 | convolution fusion | flops 100663296 | bytes 1441796 | tf_op jit(solution)/shard_map/dot_general | solution.py:12
  24.3 1.6 %collective-permute-start.14 = (f32[64,256]{1,0:T(8,128)S(1)}, f32[64,256]{1,0:T(8,128)S(1)}, u32[]{:S(2)}, u32[]{:S(2)}) collective-permute-start(f32[64,256]{1,0:T(8,128)S(1)} %get-tuple-element.59.refs_1_), channel_id=1, source_target_pairs={{0,3},{1,2},{2,1},{3,0},{4,7},{5,6},{6,5},{7,4},{8,11},{9,10},{10,... | collective-permute-start | bytes 196616 | tf_op jit(solution)/shard_map/ppermute | solution.py:33
  26.4 2.7 %collective-permute-start.12 = (f32[64,256]{1,0:T(8,128)S(1)}, f32[64,256]{1,0:T(8,128)S(1)}, u32[]{:S(2)}, u32[]{:S(2)}) collective-permute-start(f32[64,256]{1,0:T(8,128)S(1)} %get-tuple-element.59.refs_1_), channel_id=1, source_target_pairs={{0,1},{1,0},{2,3},{3,2},{4,5},{5,4},{6,7},{7,6},{8,9},{9,8},{10,11... | collective-permute-start | bytes 196616 | tf_op jit(solution)/shard_map/ppermute | solution.py:33
  29.1 0.8 constant_dynamic-update-slice_fusion.38
  30.0 0.8 constant_dynamic-update-slice_fusion.37
  30.8 0.8 constant_dynamic-update-slice_fusion.36
  31.7 1.8 %constant_dynamic-update-slice_fusion.31 = (f32[64,1024]{1,0:T(8,128)S(1)}, f32[64,256]{1,0:T(8,128)S(1)}) fusion(f32[64,1024]{1,0:T(8,128)S(1)} %broadcast.3.clone, s32[]{:T(128)S(6)} %select_n.8, f32[64,1024]{1,0:T(8,128)S(1)} %constant_dynamic-update-slice_fusion.36, f32[1,4,256,1024]{3,2,1,0:T(8,128)} %param.11), kind=kOutput, calls=%fused_computation.224 | convolution fusion | flops 100663296 | bytes 1441796 | tf_op jit(solution)/shard_map/dot_general | solution.py:12
  33.9 1.6 %collective-permute-start.8 = (f32[64,256]{1,0:T(8,128)S(1)}, f32[64,256]{1,0:T(8,128)S(1)}, u32[]{:S(2)}, u32[]{:S(2)}) collective-permute-start(f32[64,256]{1,0:T(8,128)S(1)} %get-tuple-element.51.refs_0_), channel_id=1, source_target_pairs={{0,3},{1,2},{2,1},{3,0},{4,7},{5,6},{6,5},{7,4},{8,11},{9,10},{10,... | collective-permute-start | bytes 196616 | tf_op jit(solution)/shard_map/ppermute | solution.py:33
  35.5 2.8 %collective-permute-done.6 = f32[64,256]{1,0:T(8,128)S(1)} collective-permute-done((f32[64,256]{1,0:T(8,128)S(1)}, f32[64,256]{1,0:T(8,128)S(1)}, u32[]{:S(2)}, u32[]{:S(2)}) %collective-permute-start.6) | collective-permute-done | bytes 65568 | tf_op jit(solution)/shard_map/ppermute | solution.py:33
  38.7 1.4 collective-permute-done.8
  40.4 4.8 %collective-permute-done.7 = f32[64,256]{1,0:T(8,128)S(1)} collective-permute-done((f32[64,256]{1,0:T(8,128)S(1)}, f32[64,256]{1,0:T(8,128)S(1)}, u32[]{:S(2)}, u32[]{:S(2)}) %collective-permute-start.7) | collective-permute-done | bytes 65568 | tf_op jit(solution)/shard_map/ppermute | solution.py:33
  45.8 2.1 %collective-permute-start.11 = (f32[64,256]{1,0:T(8,128)S(1)}, f32[64,256]{1,0:T(8,128)S(1)}, u32[]{:S(2)}, u32[]{:S(2)}) collective-permute-start(f32[64,256]{1,0:T(8,128)S(1)} %fusion.17), channel_id=1, source_target_pairs={{0,3},{1,2},{2,1},{3,0},{4,7},{5,6},{6,5},{7,4},{8,11},{9,10},{10,... | collective-permute-start | bytes 196616 | tf_op jit(solution)/shard_map/ppermute | solution.py:33
  47.9 2.4 %collective-permute-start.9 = (f32[64,256]{1,0:T(8,128)S(1)}, f32[64,256]{1,0:T(8,128)S(1)}, u32[]{:S(2)}, u32[]{:S(2)}) collective-permute-start(f32[64,256]{1,0:T(8,128)S(1)} %fusion.17), channel_id=1, source_target_pairs={{0,1},{1,0},{2,3},{3,2},{4,5},{5,4},{6,7},{7,6},{8,9},{9,8},{10,11... | collective-permute-start | bytes 196616 | tf_op jit(solution)/shard_map/ppermute | solution.py:33
  51.5 2.1 %collective-permute-start.17 = (f32[64,256]{1,0:T(8,128)S(1)}, f32[64,256]{1,0:T(8,128)S(1)}, u32[]{:S(2)}, u32[]{:S(2)}) collective-permute-start(f32[64,256]{1,0:T(8,128)S(1)} %fusion.14), channel_id=1, source_target_pairs={{0,3},{1,2},{2,1},{3,0},{4,7},{5,6},{6,5},{7,4},{8,11},{9,10},{10,... | collective-permute-start | bytes 196616 | tf_op jit(solution)/shard_map/ppermute | solution.py:33
  53.6 2.5 %collective-permute-start.15 = (f32[64,256]{1,0:T(8,128)S(1)}, f32[64,256]{1,0:T(8,128)S(1)}, u32[]{:S(2)}, u32[]{:S(2)}) collective-permute-start(f32[64,256]{1,0:T(8,128)S(1)} %fusion.14), channel_id=1, source_target_pairs={{0,1},{1,0},{2,3},{3,2},{4,5},{5,4},{6,7},{7,6},{8,9},{9,8},{10,11... | collective-permute-start | bytes 196616 | tf_op jit(solution)/shard_map/ppermute | solution.py:33
  57.3 2.1 %collective-permute-start.20 = (f32[64,256]{1,0:T(8,128)S(1)}, f32[64,256]{1,0:T(8,128)S(1)}, u32[]{:S(2)}, u32[]{:S(2)}) collective-permute-start(f32[64,256]{1,0:T(8,128)S(1)} %get-tuple-element.53.refs_2_), channel_id=1, source_target_pairs={{0,3},{1,2},{2,1},{3,0},{4,7},{5,6},{6,5},{7,4},{8,11},{9,10},{10,... | collective-permute-start | bytes 196616 | tf_op jit(solution)/shard_map/ppermute | solution.py:33
  59.8 2.0 %collective-permute-start.18 = (f32[64,256]{1,0:T(8,128)S(1)}, f32[64,256]{1,0:T(8,128)S(1)}, u32[]{:S(2)}, u32[]{:S(2)}) collective-permute-start(f32[64,256]{1,0:T(8,128)S(1)} %get-tuple-element.53.refs_2_), channel_id=1, source_target_pairs={{0,1},{1,0},{2,3},{3,2},{4,5},{5,4},{6,7},{7,6},{8,9},{9,8},{10,11... | collective-permute-start | bytes 196616 | tf_op jit(solution)/shard_map/ppermute | solution.py:33
  63.0 2.1 %collective-permute-start.26 = (f32[64,256]{1,0:T(8,128)S(1)}, f32[64,256]{1,0:T(8,128)S(1)}, u32[]{:S(2)}, u32[]{:S(2)}) collective-permute-start(f32[64,256]{1,0:T(8,128)S(1)} %get-tuple-element.61.refs_3_), channel_id=1, source_target_pairs={{0,3},{1,2},{2,1},{3,0},{4,7},{5,6},{6,5},{7,4},{8,11},{9,10},{10,... | collective-permute-start | bytes 196616 | tf_op jit(solution)/shard_map/ppermute | solution.py:33
  65.2 2.2 %collective-permute-start.24 = (f32[64,256]{1,0:T(8,128)S(1)}, f32[64,256]{1,0:T(8,128)S(1)}, u32[]{:S(2)}, u32[]{:S(2)}) collective-permute-start(f32[64,256]{1,0:T(8,128)S(1)} %get-tuple-element.61.refs_3_), channel_id=1, source_target_pairs={{0,1},{1,0},{2,3},{3,2},{4,5},{5,4},{6,7},{7,6},{8,9},{9,8},{10,11... | collective-permute-start | bytes 196616 | tf_op jit(solution)/shard_map/ppermute | solution.py:33
  68.6 2.1 %collective-permute-start.23 = (f32[64,256]{1,0:T(8,128)S(1)}, f32[64,256]{1,0:T(8,128)S(1)}, u32[]{:S(2)}, u32[]{:S(2)}) collective-permute-start(f32[64,256]{1,0:T(8,128)S(1)} %fusion.11), channel_id=1, source_target_pairs={{0,3},{1,2},{2,1},{3,0},{4,7},{5,6},{6,5},{7,4},{8,11},{9,10},{10,... | collective-permute-start | bytes 196616 | tf_op jit(solution)/shard_map/ppermute | solution.py:33
  70.7 2.4 %collective-permute-start.21 = (f32[64,256]{1,0:T(8,128)S(1)}, f32[64,256]{1,0:T(8,128)S(1)}, u32[]{:S(2)}, u32[]{:S(2)}) collective-permute-start(f32[64,256]{1,0:T(8,128)S(1)} %fusion.11), channel_id=1, source_target_pairs={{0,1},{1,0},{2,3},{3,2},{4,5},{5,4},{6,7},{7,6},{8,9},{9,8},{10,11... | collective-permute-start | bytes 196616 | tf_op jit(solution)/shard_map/ppermute | solution.py:33
  74.4 2.0 %collective-permute-start.29 = (f32[64,256]{1,0:T(8,128)S(1)}, f32[64,256]{1,0:T(8,128)S(1)}, u32[]{:S(2)}, u32[]{:S(2)}) collective-permute-start(f32[64,256]{1,0:T(8,128)S(1)} %fusion.8), channel_id=1, source_target_pairs={{0,3},{1,2},{2,1},{3,0},{4,7},{5,6},{6,5},{7,4},{8,11},{9,10},{10,... | collective-permute-start | bytes 196616 | tf_op jit(solution)/shard_map/ppermute | solution.py:33
  76.5 2.6 %collective-permute-start.27 = (f32[64,256]{1,0:T(8,128)S(1)}, f32[64,256]{1,0:T(8,128)S(1)}, u32[]{:S(2)}, u32[]{:S(2)}) collective-permute-start(f32[64,256]{1,0:T(8,128)S(1)} %fusion.8), channel_id=1, source_target_pairs={{0,1},{1,0},{2,3},{3,2},{4,5},{5,4},{6,7},{7,6},{8,9},{9,8},{10,11... | collective-permute-start | bytes 196616 | tf_op jit(solution)/shard_map/ppermute | solution.py:33
  80.2 2.0 %collective-permute-start.32 = (f32[64,256]{1,0:T(8,128)S(1)}, f32[64,256]{1,0:T(8,128)S(1)}, u32[]{:S(2)}, u32[]{:S(2)}) collective-permute-start(f32[64,256]{1,0:T(8,128)S(1)} %get-tuple-element.55.refs_4_), channel_id=1, source_target_pairs={{0,3},{1,2},{2,1},{3,0},{4,7},{5,6},{6,5},{7,4},{8,11},{9,10},{10,... | collective-permute-start | bytes 196616 | tf_op jit(solution)/shard_map/ppermute | solution.py:33
  82.2 2.5 %collective-permute-start.30 = (f32[64,256]{1,0:T(8,128)S(1)}, f32[64,256]{1,0:T(8,128)S(1)}, u32[]{:S(2)}, u32[]{:S(2)}) collective-permute-start(f32[64,256]{1,0:T(8,128)S(1)} %get-tuple-element.55.refs_4_), channel_id=1, source_target_pairs={{0,1},{1,0},{2,3},{3,2},{4,5},{5,4},{6,7},{7,6},{8,9},{9,8},{10,11... | collective-permute-start | bytes 196616 | tf_op jit(solution)/shard_map/ppermute | solution.py:33
  85.9 2.0 %collective-permute-start.38 = (f32[64,256]{1,0:T(8,128)S(1)}, f32[64,256]{1,0:T(8,128)S(1)}, u32[]{:S(2)}, u32[]{:S(2)}) collective-permute-start(f32[64,256]{1,0:T(8,128)S(1)} %get-tuple-element.63.refs_5_), channel_id=1, source_target_pairs={{0,3},{1,2},{2,1},{3,0},{4,7},{5,6},{6,5},{7,4},{8,11},{9,10},{10,... | collective-permute-start | bytes 196616 | tf_op jit(solution)/shard_map/ppermute | solution.py:33
  87.9 2.5 %collective-permute-start.36 = (f32[64,256]{1,0:T(8,128)S(1)}, f32[64,256]{1,0:T(8,128)S(1)}, u32[]{:S(2)}, u32[]{:S(2)}) collective-permute-start(f32[64,256]{1,0:T(8,128)S(1)} %get-tuple-element.63.refs_5_), channel_id=1, source_target_pairs={{0,1},{1,0},{2,3},{3,2},{4,5},{5,4},{6,7},{7,6},{8,9},{9,8},{10,11... | collective-permute-start | bytes 196616 | tf_op jit(solution)/shard_map/ppermute | solution.py:33
  91.6 2.0 %collective-permute-start.35 = (f32[64,256]{1,0:T(8,128)S(1)}, f32[64,256]{1,0:T(8,128)S(1)}, u32[]{:S(2)}, u32[]{:S(2)}) collective-permute-start(f32[64,256]{1,0:T(8,128)S(1)} %fusion.5), channel_id=1, source_target_pairs={{0,3},{1,2},{2,1},{3,0},{4,7},{5,6},{6,5},{7,4},{8,11},{9,10},{10,... | collective-permute-start | bytes 196616 | tf_op jit(solution)/shard_map/ppermute | solution.py:33
  93.6 2.5 %collective-permute-start.33 = (f32[64,256]{1,0:T(8,128)S(1)}, f32[64,256]{1,0:T(8,128)S(1)}, u32[]{:S(2)}, u32[]{:S(2)}) collective-permute-start(f32[64,256]{1,0:T(8,128)S(1)} %fusion.5), channel_id=1, source_target_pairs={{0,1},{1,0},{2,3},{3,2},{4,5},{5,4},{6,7},{7,6},{8,9},{9,8},{10,11... | collective-permute-start | bytes 196616 | tf_op jit(solution)/shard_map/ppermute | solution.py:33
  97.3 2.0 %collective-permute-start.41 = (f32[64,256]{1,0:T(8,128)S(1)}, f32[64,256]{1,0:T(8,128)S(1)}, u32[]{:S(2)}, u32[]{:S(2)}) collective-permute-start(f32[64,256]{1,0:T(8,128)S(1)} %fusion.2), channel_id=1, source_target_pairs={{0,3},{1,2},{2,1},{3,0},{4,7},{5,6},{6,5},{7,4},{8,11},{9,10},{10,... | collective-permute-start | bytes 196616 | tf_op jit(solution)/shard_map/ppermute | solution.py:33
  99.3 2.6 %collective-permute-start.39 = (f32[64,256]{1,0:T(8,128)S(1)}, f32[64,256]{1,0:T(8,128)S(1)}, u32[]{:S(2)}, u32[]{:S(2)}) collective-permute-start(f32[64,256]{1,0:T(8,128)S(1)} %fusion.2), channel_id=1, source_target_pairs={{0,1},{1,0},{2,3},{3,2},{4,5},{5,4},{6,7},{7,6},{8,9},{9,8},{10,11... | collective-permute-start | bytes 196616 | tf_op jit(solution)/shard_map/ppermute | solution.py:33
  102.8 2.0 %collective-permute-start.44 = (f32[64,256]{1,0:T(8,128)S(1)}, f32[64,256]{1,0:T(8,128)S(1)}, u32[]{:S(2)}, u32[]{:S(2)}) collective-permute-start(f32[64,256]{1,0:T(8,128)S(1)} %get-tuple-element.57.refs_6_), channel_id=1, source_target_pairs={{0,3},{1,2},{2,1},{3,0},{4,7},{5,6},{6,5},{7,4},{8,11},{9,10},{10,... | collective-permute-start | bytes 196616 | tf_op jit(solution)/shard_map/ppermute | solution.py:33
  104.8 2.5 %collective-permute-start.42 = (f32[64,256]{1,0:T(8,128)S(1)}, f32[64,256]{1,0:T(8,128)S(1)}, u32[]{:S(2)}, u32[]{:S(2)}) collective-permute-start(f32[64,256]{1,0:T(8,128)S(1)} %get-tuple-element.57.refs_6_), channel_id=1, source_target_pairs={{0,1},{1,0},{2,3},{3,2},{4,5},{5,4},{6,7},{7,6},{8,9},{9,8},{10,11... | collective-permute-start | bytes 196616 | tf_op jit(solution)/shard_map/ppermute | solution.py:33
  108.2 2.0 %collective-permute-start.47 = (f32[64,256]{1,0:T(8,128)S(1)}, f32[64,256]{1,0:T(8,128)S(1)}, u32[]{:S(2)}, u32[]{:S(2)}) collective-permute-start(f32[64,256]{1,0:T(8,128)S(1)} %get-tuple-element.65.refs_7_), channel_id=1, source_target_pairs={{0,3},{1,2},{2,1},{3,0},{4,7},{5,6},{6,5},{7,4},{8,11},{9,10},{10,... | collective-permute-start | bytes 196616 | tf_op jit(solution)/shard_map/ppermute | solution.py:33
  110.2 2.5 %collective-permute-start.45 = (f32[64,256]{1,0:T(8,128)S(1)}, f32[64,256]{1,0:T(8,128)S(1)}, u32[]{:S(2)}, u32[]{:S(2)}) collective-permute-start(f32[64,256]{1,0:T(8,128)S(1)} %get-tuple-element.65.refs_7_), channel_id=1, source_target_pairs={{0,1},{1,0},{2,3},{3,2},{4,5},{5,4},{6,7},{7,6},{8,9},{9,8},{10,11... | collective-permute-start | bytes 196616 | tf_op jit(solution)/shard_map/ppermute | solution.py:33
  112.8 1.7 %shard_map.115.refs_0_ = f32[64,384]{1,0:T(8,128)S(1)} custom-call(f32[64,1024]{1,0:T(8,128)S(1)} %constant_dynamic-update-slice_fusion.28.refs_0_, f32[64,1024]{1,0:T(8,128)S(1)} %constant_dynamic-update-slice_fusion.24.refs_1_, f32[64,1024]{1,0:T(8,128)S(1)} %constant_dynamic-update-slice_fusion.20.refs_2_, ...), custom_call_target="tpu_custom_call" | custom-call | flops 150994944 | bytes 2719756 | tf_op jit(solution)/shard_map/pallas_call | solution.py:80
  115.8 1.5 shard_map.116
  117.4 1.3 collective-permute-done.48.refs_1_
  118.8 1.6 %collective-permute-start.49 = (f32[2,16,512]{2,1,0:T(8,128)S(1)}, f32[2,16,512]{2,1,0:T(8,128)S(1)}, u32[]{:S(2)}, u32[]{:S(2)}) collective-permute-start(f32[2,16,512]{2,1,0:T(8,128)S(1)} %get-tuple-element.37), channel_id=1, source_target_pairs={{0,8},{4,12},{8,0},{12,4},{16,24},{20,28},{24,16},{28,20},{1,9},{5... | collective-permute-start | bytes 196616 | tf_op jit(solution)/shard_map/ppermute | solution.py:71
  120.3 1.5 collective-permute-start.50
  122.3 1.0 shard_map.117.refs_5_
  123.3 1.3 collective-permute-done.50.refs_2_
  124.6 2.4 %collective-permute-done.51.refs_3_ = f32[2,16,512]{2,1,0:T(8,128)S(1)} collective-permute-done((f32[2,16,512]{2,1,0:T(8,128)S(1)}, f32[2,16,512]{2,1,0:T(8,128)S(1)}, u32[]{:S(2)}, u32[]{:S(2)}) %collective-permute-start.51) | collective-permute-done | bytes 65568 | tf_op jit(solution)/shard_map/ppermute | solution.py:71
  127.0 1.0 copy-done.3
  128.4 1.3 collective-permute-start.52
  129.7 1.2 collective-permute-start.53
  131.0 1.9 %collective-permute-start.54 = (f32[16,1280]{1,0:T(8,128)S(1)}, f32[16,1280]{1,0:T(8,128)S(1)}, u32[]{:S(2)}, u32[]{:S(2)}) collective-permute-start(f32[16,1280]{1,0:T(8,128)S(1)} %get-tuple-element.43), channel_id=1, source_target_pairs={{0,3},{1,2},{2,1},{3,0},{4,7},{5,6},{6,5},{7,4},{8,11},{9,10},{10,... | collective-permute-start | bytes 245768 | tf_op jit(solution)/shard_map/ppermute | solution.py:33
  133.7 3.8 %collective-permute-done.53.refs_2_ = f32[16,1280]{1,0:T(8,128)S(1)} collective-permute-done((f32[16,1280]{1,0:T(8,128)S(1)}, f32[16,1280]{1,0:T(8,128)S(1)}, u32[]{:S(2)}, u32[]{:S(2)}) %collective-permute-start.53) | collective-permute-done | bytes 81952 | tf_op jit(solution)/shard_map/ppermute | solution.py:33
  138.0 1.9 %collective-permute-start.57 = (f32[16,256]{1,0:T(8,128)S(1)}, f32[16,256]{1,0:T(8,128)S(1)}, u32[]{:S(2)}, u32[]{:S(2)}) collective-permute-start(f32[16,256]{1,0:T(8,128)S(1)} %get-tuple-element.46.refs_0_), channel_id=1, source_target_pairs={{0,3},{1,2},{2,1},{3,0},{4,7},{5,6},{6,5},{7,4},{8,11},{9,10},{10,... | collective-permute-start | bytes 49160 | tf_op jit(solution)/shard_map/ppermute | solution.py:33
  139.9 1.0 collective-permute-start.56
  141.0 1.5 collective-permute-start.55
  142.4 1.1 collective-permute-done.57.refs_3_
  143.6 1.3 collective-permute-done.56.refs_2_
  145.4 2.0 %collective-permute-start.60 = (f32[16,256]{1,0:T(8,128)S(1)}, f32[16,256]{1,0:T(8,128)S(1)}, u32[]{:S(2)}, u32[]{:S(2)}) collective-permute-start(f32[16,256]{1,0:T(8,128)S(1)} %shard_map.122.refs_0_), channel_id=1, source_target_pairs={{0,3},{1,2},{2,1},{3,0},{4,7},{5,6},{6,5},{7,4},{8,11},{9,10},{10,... | collective-permute-start | bytes 49160 | tf_op jit(solution)/shard_map/ppermute | solution.py:33
  148.2 1.6 %collective-permute-start.58 = (f32[16,256]{1,0:T(8,128)S(1)}, f32[16,256]{1,0:T(8,128)S(1)}, u32[]{:S(2)}, u32[]{:S(2)}) collective-permute-start(f32[16,256]{1,0:T(8,128)S(1)} %shard_map.122.refs_0_), channel_id=1, source_target_pairs={{0,1},{1,0},{2,3},{3,2},{4,5},{5,4},{6,7},{7,6},{8,9},{9,8},{10,11... | collective-permute-start | bytes 49160 | tf_op jit(solution)/shard_map/ppermute | solution.py:33
  149.8 1.1 collective-permute-done.60.refs_3_
  151.0 1.2 collective-permute-done.59.refs_2_
  (190 shorter events, 24.9 us)
Async XLA Ops:
  1.8 29.0 %collective-permute-start.2 = (f32[64,256]{1,0:T(8,128)S(1)}, f32[64,256]{1,0:T(8,128)}, u32[]{:S(2)}, u32[]{:S(2)}) collective-permute-start(f32[64,256]{1,0:T(8,128)S(1)} %get-tuple-element.26), channel_id=1, source_target_pairs={{0,3},{1,2},{2,1},{3,0},{4,7},{5,6},{6,5},{7,4},{8,11},{9,10},{10,... | collective-permute-start | bytes 196616 | tf_op jit(solution)/shard_map/ppermute | solution.py:33
  6.9 23.0 %collective-permute-start.1 = (f32[64,256]{1,0:T(8,128)S(1)}, f32[64,256]{1,0:T(8,128)}, u32[]{:S(2)}, u32[]{:S(2)}) collective-permute-start(f32[64,256]{1,0:T(8,128)S(1)} %get-tuple-element.26), channel_id=1, source_target_pairs={{0,2},{1,3},{2,0},{3,1},{4,6},{5,7},{6,4},{7,5},{8,10},{9,11},{10,... | collective-permute-start | bytes 196616 | tf_op jit(solution)/shard_map/ppermute | solution.py:33
  6.9 19.5 %collective-permute-start = (f32[64,256]{1,0:T(8,128)S(1)}, f32[64,256]{1,0:T(8,128)}, u32[]{:S(2)}, u32[]{:S(2)}) collective-permute-start(f32[64,256]{1,0:T(8,128)S(1)} %get-tuple-element.26), channel_id=1, source_target_pairs={{0,1},{1,0},{2,3},{3,2},{4,5},{5,4},{6,7},{7,6},{8,9},{9,8},{10,11... | collective-permute-start | bytes 196616 | tf_op jit(solution)/shard_map/ppermute | solution.py:33
  7.6 14.0 %collective-permute-start.5 = (f32[64,256]{1,0:T(8,128)S(1)}, f32[64,256]{1,0:T(8,128)}, u32[]{:S(2)}, u32[]{:S(2)}) collective-permute-start(f32[64,256]{1,0:T(8,128)S(1)} %get-tuple-element.27), channel_id=1, source_target_pairs={{0,3},{1,2},{2,1},{3,0},{4,7},{5,6},{6,5},{7,4},{8,11},{9,10},{10,... | collective-permute-start | bytes 196616 | tf_op jit(solution)/shard_map/ppermute | solution.py:33
  11.3 4.4 %collective-permute-start.3 = (f32[64,256]{1,0:T(8,128)S(1)}, f32[64,256]{1,0:T(8,128)}, u32[]{:S(2)}, u32[]{:S(2)}) collective-permute-start(f32[64,256]{1,0:T(8,128)S(1)} %get-tuple-element.27), channel_id=1, source_target_pairs={{0,1},{1,0},{2,3},{3,2},{4,5},{5,4},{6,7},{7,6},{8,9},{9,8},{10,11... | collective-permute-start | bytes 196616 | tf_op jit(solution)/shard_map/ppermute | solution.py:33
  14.4 30.8 %copy-start.8 = (f32[64,256]{1,0:T(8,128)S(1)}, f32[64,256]{1,0:T(8,128)}, u32[]{:S(2)}) copy-start(f32[64,256]{1,0:T(8,128)} %copy-done.7) | copy-start | bytes 196612
  14.4 31.1 %copy-start.12 = (f32[1,4,256,1024]{3,2,1,0:T(8,128)S(1)}, f32[1,4,256,1024]{3,2,1,0:T(8,128)}, u32[]{:S(2)}) copy-start(f32[1,4,256,1024]{3,2,1,0:T(8,128)} %param.11) | copy-start | bytes 12582916
  14.4 36.5 %copy-start.6 = (f32[64,256]{1,0:T(8,128)S(1)}, f32[64,256]{1,0:T(8,128)}, u32[]{:S(2)}) copy-start(f32[64,256]{1,0:T(8,128)} %copy-done.5) | copy-start | bytes 196612
  15.7 5.9 %collective-permute-start.4 = (f32[64,256]{1,0:T(8,128)S(1)}, f32[64,256]{1,0:T(8,128)S(1)}, u32[]{:S(2)}, u32[]{:S(2)}) collective-permute-start(f32[64,256]{1,0:T(8,128)S(1)} %get-tuple-element.27), channel_id=1, source_target_pairs={{0,2},{1,3},{2,0},{3,1},{4,6},{5,7},{6,4},{7,5},{8,10},{9,11},{10,... | collective-permute-start | bytes 196616 | tf_op jit(solution)/shard_map/ppermute | solution.py:33
  24.3 26.3 %collective-permute-start.14 = (f32[64,256]{1,0:T(8,128)S(1)}, f32[64,256]{1,0:T(8,128)S(1)}, u32[]{:S(2)}, u32[]{:S(2)}) collective-permute-start(f32[64,256]{1,0:T(8,128)S(1)} %get-tuple-element.59.refs_1_), channel_id=1, source_target_pairs={{0,3},{1,2},{2,1},{3,0},{4,7},{5,6},{6,5},{7,4},{8,11},{9,10},{10,... | collective-permute-start | bytes 196616 | tf_op jit(solution)/shard_map/ppermute | solution.py:33
  25.9 25.0 %collective-permute-start.13 = (f32[64,256]{1,0:T(8,128)S(1)}, f32[64,256]{1,0:T(8,128)S(1)}, u32[]{:S(2)}, u32[]{:S(2)}) collective-permute-start(f32[64,256]{1,0:T(8,128)S(1)} %get-tuple-element.59.refs_1_), channel_id=1, source_target_pairs={{0,2},{1,3},{2,0},{3,1},{4,6},{5,7},{6,4},{7,5},{8,10},{9,11},{10,... | collective-permute-start | bytes 196616 | tf_op jit(solution)/shard_map/ppermute | solution.py:33
  26.4 21.4 %collective-permute-start.12 = (f32[64,256]{1,0:T(8,128)S(1)}, f32[64,256]{1,0:T(8,128)S(1)}, u32[]{:S(2)}, u32[]{:S(2)}) collective-permute-start(f32[64,256]{1,0:T(8,128)S(1)} %get-tuple-element.59.refs_1_), channel_id=1, source_target_pairs={{0,1},{1,0},{2,3},{3,2},{4,5},{5,4},{6,7},{7,6},{8,9},{9,8},{10,11... | collective-permute-start | bytes 196616 | tf_op jit(solution)/shard_map/ppermute | solution.py:33
  33.5 4.7 %collective-permute-start.6 = (f32[64,256]{1,0:T(8,128)S(1)}, f32[64,256]{1,0:T(8,128)S(1)}, u32[]{:S(2)}, u32[]{:S(2)}) collective-permute-start(f32[64,256]{1,0:T(8,128)S(1)} %get-tuple-element.51.refs_0_), channel_id=1, source_target_pairs={{0,1},{1,0},{2,3},{3,2},{4,5},{5,4},{6,7},{7,6},{8,9},{9,8},{10,11... | collective-permute-start | bytes 196616 | tf_op jit(solution)/shard_map/ppermute | solution.py:33
  33.9 6.2 %collective-permute-start.8 = (f32[64,256]{1,0:T(8,128)S(1)}, f32[64,256]{1,0:T(8,128)S(1)}, u32[]{:S(2)}, u32[]{:S(2)}) collective-permute-start(f32[64,256]{1,0:T(8,128)S(1)} %get-tuple-element.51.refs_0_), channel_id=1, source_target_pairs={{0,3},{1,2},{2,1},{3,0},{4,7},{5,6},{6,5},{7,4},{8,11},{9,10},{10,... | collective-permute-start | bytes 196616 | tf_op jit(solution)/shard_map/ppermute | solution.py:33
  38.2 7.0 %collective-permute-start.7 = (f32[64,256]{1,0:T(8,128)S(1)}, f32[64,256]{1,0:T(8,128)S(1)}, u32[]{:S(2)}, u32[]{:S(2)}) collective-permute-start(f32[64,256]{1,0:T(8,128)S(1)} %get-tuple-element.51.refs_0_), channel_id=1, source_target_pairs={{0,2},{1,3},{2,0},{3,1},{4,6},{5,7},{6,4},{7,5},{8,10},{9,11},{10,... | collective-permute-start | bytes 196616 | tf_op jit(solution)/shard_map/ppermute | solution.py:33
  45.8 10.6 %collective-permute-start.11 = (f32[64,256]{1,0:T(8,128)S(1)}, f32[64,256]{1,0:T(8,128)S(1)}, u32[]{:S(2)}, u32[]{:S(2)}) collective-permute-start(f32[64,256]{1,0:T(8,128)S(1)} %fusion.17), channel_id=1, source_target_pairs={{0,3},{1,2},{2,1},{3,0},{4,7},{5,6},{6,5},{7,4},{8,11},{9,10},{10,... | collective-permute-start | bytes 196616 | tf_op jit(solution)/shard_map/ppermute | solution.py:33
  47.9 8.8 %collective-permute-start.10 = (f32[64,256]{1,0:T(8,128)S(1)}, f32[64,256]{1,0:T(8,128)S(1)}, u32[]{:S(2)}, u32[]{:S(2)}) collective-permute-start(f32[64,256]{1,0:T(8,128)S(1)} %fusion.17), channel_id=1, source_target_pairs={{0,2},{1,3},{2,0},{3,1},{4,6},{5,7},{6,4},{7,5},{8,10},{9,11},{10,... | collective-permute-start | bytes 196616 | tf_op jit(solution)/shard_map/ppermute | solution.py:33
  47.9 5.8 %collective-permute-start.9 = (f32[64,256]{1,0:T(8,128)S(1)}, f32[64,256]{1,0:T(8,128)S(1)}, u32[]{:S(2)}, u32[]{:S(2)}) collective-permute-start(f32[64,256]{1,0:T(8,128)S(1)} %fusion.17), channel_id=1, source_target_pairs={{0,1},{1,0},{2,3},{3,2},{4,5},{5,4},{6,7},{7,6},{8,9},{9,8},{10,11... | collective-permute-start | bytes 196616 | tf_op jit(solution)/shard_map/ppermute | solution.py:33
  51.5 10.6 %collective-permute-start.17 = (f32[64,256]{1,0:T(8,128)S(1)}, f32[64,256]{1,0:T(8,128)S(1)}, u32[]{:S(2)}, u32[]{:S(2)}) collective-permute-start(f32[64,256]{1,0:T(8,128)S(1)} %fusion.14), channel_id=1, source_target_pairs={{0,3},{1,2},{2,1},{3,0},{4,7},{5,6},{6,5},{7,4},{8,11},{9,10},{10,... | collective-permute-start | bytes 196616 | tf_op jit(solution)/shard_map/ppermute | solution.py:33
  53.5 8.9 %collective-permute-start.16 = (f32[64,256]{1,0:T(8,128)S(1)}, f32[64,256]{1,0:T(8,128)S(1)}, u32[]{:S(2)}, u32[]{:S(2)}) collective-permute-start(f32[64,256]{1,0:T(8,128)S(1)} %fusion.14), channel_id=1, source_target_pairs={{0,2},{1,3},{2,0},{3,1},{4,6},{5,7},{6,4},{7,5},{8,10},{9,11},{10,... | collective-permute-start | bytes 196616 | tf_op jit(solution)/shard_map/ppermute | solution.py:33
  53.6 6.1 %collective-permute-start.15 = (f32[64,256]{1,0:T(8,128)S(1)}, f32[64,256]{1,0:T(8,128)S(1)}, u32[]{:S(2)}, u32[]{:S(2)}) collective-permute-start(f32[64,256]{1,0:T(8,128)S(1)} %fusion.14), channel_id=1, source_target_pairs={{0,1},{1,0},{2,3},{3,2},{4,5},{5,4},{6,7},{7,6},{8,9},{9,8},{10,11... | collective-permute-start | bytes 196616 | tf_op jit(solution)/shard_map/ppermute | solution.py:33
  57.3 10.4 %collective-permute-start.20 = (f32[64,256]{1,0:T(8,128)S(1)}, f32[64,256]{1,0:T(8,128)S(1)}, u32[]{:S(2)}, u32[]{:S(2)}) collective-permute-start(f32[64,256]{1,0:T(8,128)S(1)} %get-tuple-element.53.refs_2_), channel_id=1, source_target_pairs={{0,3},{1,2},{2,1},{3,0},{4,7},{5,6},{6,5},{7,4},{8,11},{9,10},{10,... | collective-permute-start | bytes 196616 | tf_op jit(solution)/shard_map/ppermute | solution.py:33
  59.4 8.7 %collective-permute-start.19 = (f32[64,256]{1,0:T(8,128)S(1)}, f32[64,256]{1,0:T(8,128)S(1)}, u32[]{:S(2)}, u32[]{:S(2)}) collective-permute-start(f32[64,256]{1,0:T(8,128)S(1)} %get-tuple-element.53.refs_2_), channel_id=1, source_target_pairs={{0,2},{1,3},{2,0},{3,1},{4,6},{5,7},{6,4},{7,5},{8,10},{9,11},{10,... | collective-permute-start | bytes 196616 | tf_op jit(solution)/shard_map/ppermute | solution.py:33
  59.8 5.5 %collective-permute-start.18 = (f32[64,256]{1,0:T(8,128)S(1)}, f32[64,256]{1,0:T(8,128)S(1)}, u32[]{:S(2)}, u32[]{:S(2)}) collective-permute-start(f32[64,256]{1,0:T(8,128)S(1)} %get-tuple-element.53.refs_2_), channel_id=1, source_target_pairs={{0,1},{1,0},{2,3},{3,2},{4,5},{5,4},{6,7},{7,6},{8,9},{9,8},{10,11... | collective-permute-start | bytes 196616 | tf_op jit(solution)/shard_map/ppermute | solution.py:33
  63.0 10.4 %collective-permute-start.26 = (f32[64,256]{1,0:T(8,128)S(1)}, f32[64,256]{1,0:T(8,128)S(1)}, u32[]{:S(2)}, u32[]{:S(2)}) collective-permute-start(f32[64,256]{1,0:T(8,128)S(1)} %get-tuple-element.61.refs_3_), channel_id=1, source_target_pairs={{0,3},{1,2},{2,1},{3,0},{4,7},{5,6},{6,5},{7,4},{8,11},{9,10},{10,... | collective-permute-start | bytes 196616 | tf_op jit(solution)/shard_map/ppermute | solution.py:33
  65.0 8.8 %collective-permute-start.25 = (f32[64,256]{1,0:T(8,128)S(1)}, f32[64,256]{1,0:T(8,128)S(1)}, u32[]{:S(2)}, u32[]{:S(2)}) collective-permute-start(f32[64,256]{1,0:T(8,128)S(1)} %get-tuple-element.61.refs_3_), channel_id=1, source_target_pairs={{0,2},{1,3},{2,0},{3,1},{4,6},{5,7},{6,4},{7,5},{8,10},{9,11},{10,... | collective-permute-start | bytes 196616 | tf_op jit(solution)/shard_map/ppermute | solution.py:33
  65.2 5.5 %collective-permute-start.24 = (f32[64,256]{1,0:T(8,128)S(1)}, f32[64,256]{1,0:T(8,128)S(1)}, u32[]{:S(2)}, u32[]{:S(2)}) collective-permute-start(f32[64,256]{1,0:T(8,128)S(1)} %get-tuple-element.61.refs_3_), channel_id=1, source_target_pairs={{0,1},{1,0},{2,3},{3,2},{4,5},{5,4},{6,7},{7,6},{8,9},{9,8},{10,11... | collective-permute-start | bytes 196616 | tf_op jit(solution)/shard_map/ppermute | solution.py:33
  68.6 10.7 %collective-permute-start.23 = (f32[64,256]{1,0:T(8,128)S(1)}, f32[64,256]{1,0:T(8,128)S(1)}, u32[]{:S(2)}, u32[]{:S(2)}) collective-permute-start(f32[64,256]{1,0:T(8,128)S(1)} %fusion.11), channel_id=1, source_target_pairs={{0,3},{1,2},{2,1},{3,0},{4,7},{5,6},{6,5},{7,4},{8,11},{9,10},{10,... | collective-permute-start | bytes 196616 | tf_op jit(solution)/shard_map/ppermute | solution.py:33
  70.7 8.9 %collective-permute-start.22 = (f32[64,256]{1,0:T(8,128)S(1)}, f32[64,256]{1,0:T(8,128)S(1)}, u32[]{:S(2)}, u32[]{:S(2)}) collective-permute-start(f32[64,256]{1,0:T(8,128)S(1)} %fusion.11), channel_id=1, source_target_pairs={{0,2},{1,3},{2,0},{3,1},{4,6},{5,7},{6,4},{7,5},{8,10},{9,11},{10,... | collective-permute-start | bytes 196616 | tf_op jit(solution)/shard_map/ppermute | solution.py:33
  70.7 5.8 %collective-permute-start.21 = (f32[64,256]{1,0:T(8,128)S(1)}, f32[64,256]{1,0:T(8,128)S(1)}, u32[]{:S(2)}, u32[]{:S(2)}) collective-permute-start(f32[64,256]{1,0:T(8,128)S(1)} %fusion.11), channel_id=1, source_target_pairs={{0,1},{1,0},{2,3},{3,2},{4,5},{5,4},{6,7},{7,6},{8,9},{9,8},{10,11... | collective-permute-start | bytes 196616 | tf_op jit(solution)/shard_map/ppermute | solution.py:33
  74.4 10.6 %collective-permute-start.29 = (f32[64,256]{1,0:T(8,128)S(1)}, f32[64,256]{1,0:T(8,128)S(1)}, u32[]{:S(2)}, u32[]{:S(2)}) collective-permute-start(f32[64,256]{1,0:T(8,128)S(1)} %fusion.8), channel_id=1, source_target_pairs={{0,3},{1,2},{2,1},{3,0},{4,7},{5,6},{6,5},{7,4},{8,11},{9,10},{10,... | collective-permute-start | bytes 196616 | tf_op jit(solution)/shard_map/ppermute | solution.py:33
  76.4 8.9 %collective-permute-start.28 = (f32[64,256]{1,0:T(8,128)S(1)}, f32[64,256]{1,0:T(8,128)S(1)}, u32[]{:S(2)}, u32[]{:S(2)}) collective-permute-start(f32[64,256]{1,0:T(8,128)S(1)} %fusion.8), channel_id=1, source_target_pairs={{0,2},{1,3},{2,0},{3,1},{4,6},{5,7},{6,4},{7,5},{8,10},{9,11},{10,... | collective-permute-start | bytes 196616 | tf_op jit(solution)/shard_map/ppermute | solution.py:33
  76.5 5.7 %collective-permute-start.27 = (f32[64,256]{1,0:T(8,128)S(1)}, f32[64,256]{1,0:T(8,128)S(1)}, u32[]{:S(2)}, u32[]{:S(2)}) collective-permute-start(f32[64,256]{1,0:T(8,128)S(1)} %fusion.8), channel_id=1, source_target_pairs={{0,1},{1,0},{2,3},{3,2},{4,5},{5,4},{6,7},{7,6},{8,9},{9,8},{10,11... | collective-permute-start | bytes 196616 | tf_op jit(solution)/shard_map/ppermute | solution.py:33
  80.2 10.4 %collective-permute-start.32 = (f32[64,256]{1,0:T(8,128)S(1)}, f32[64,256]{1,0:T(8,128)S(1)}, u32[]{:S(2)}, u32[]{:S(2)}) collective-permute-start(f32[64,256]{1,0:T(8,128)S(1)} %get-tuple-element.55.refs_4_), channel_id=1, source_target_pairs={{0,3},{1,2},{2,1},{3,0},{4,7},{5,6},{6,5},{7,4},{8,11},{9,10},{10,... | collective-permute-start | bytes 196616 | tf_op jit(solution)/shard_map/ppermute | solution.py:33
  82.2 8.8 %collective-permute-start.31 = (f32[64,256]{1,0:T(8,128)S(1)}, f32[64,256]{1,0:T(8,128)S(1)}, u32[]{:S(2)}, u32[]{:S(2)}) collective-permute-start(f32[64,256]{1,0:T(8,128)S(1)} %get-tuple-element.55.refs_4_), channel_id=1, source_target_pairs={{0,2},{1,3},{2,0},{3,1},{4,6},{5,7},{6,4},{7,5},{8,10},{9,11},{10,... | collective-permute-start | bytes 196616 | tf_op jit(solution)/shard_map/ppermute | solution.py:33
  82.2 5.7 %collective-permute-start.30 = (f32[64,256]{1,0:T(8,128)S(1)}, f32[64,256]{1,0:T(8,128)S(1)}, u32[]{:S(2)}, u32[]{:S(2)}) collective-permute-start(f32[64,256]{1,0:T(8,128)S(1)} %get-tuple-element.55.refs_4_), channel_id=1, source_target_pairs={{0,1},{1,0},{2,3},{3,2},{4,5},{5,4},{6,7},{7,6},{8,9},{9,8},{10,11... | collective-permute-start | bytes 196616 | tf_op jit(solution)/shard_map/ppermute | solution.py:33
  85.9 10.4 %collective-permute-start.38 = (f32[64,256]{1,0:T(8,128)S(1)}, f32[64,256]{1,0:T(8,128)S(1)}, u32[]{:S(2)}, u32[]{:S(2)}) collective-permute-start(f32[64,256]{1,0:T(8,128)S(1)} %get-tuple-element.63.refs_5_), channel_id=1, source_target_pairs={{0,3},{1,2},{2,1},{3,0},{4,7},{5,6},{6,5},{7,4},{8,11},{9,10},{10,... | collective-permute-start | bytes 196616 | tf_op jit(solution)/shard_map/ppermute | solution.py:33
  87.9 8.7 %collective-permute-start.37 = (f32[64,256]{1,0:T(8,128)S(1)}, f32[64,256]{1,0:T(8,128)S(1)}, u32[]{:S(2)}, u32[]{:S(2)}) collective-permute-start(f32[64,256]{1,0:T(8,128)S(1)} %get-tuple-element.63.refs_5_), channel_id=1, source_target_pairs={{0,2},{1,3},{2,0},{3,1},{4,6},{5,7},{6,4},{7,5},{8,10},{9,11},{10,... | collective-permute-start | bytes 196616 | tf_op jit(solution)/shard_map/ppermute | solution.py:33
  87.9 5.6 %collective-permute-start.36 = (f32[64,256]{1,0:T(8,128)S(1)}, f32[64,256]{1,0:T(8,128)S(1)}, u32[]{:S(2)}, u32[]{:S(2)}) collective-permute-start(f32[64,256]{1,0:T(8,128)S(1)} %get-tuple-element.63.refs_5_), channel_id=1, source_target_pairs={{0,1},{1,0},{2,3},{3,2},{4,5},{5,4},{6,7},{7,6},{8,9},{9,8},{10,11... | collective-permute-start | bytes 196616 | tf_op jit(solution)/shard_map/ppermute | solution.py:33
  91.6 10.6 %collective-permute-start.35 = (f32[64,256]{1,0:T(8,128)S(1)}, f32[64,256]{1,0:T(8,128)S(1)}, u32[]{:S(2)}, u32[]{:S(2)}) collective-permute-start(f32[64,256]{1,0:T(8,128)S(1)} %fusion.5), channel_id=1, source_target_pairs={{0,3},{1,2},{2,1},{3,0},{4,7},{5,6},{6,5},{7,4},{8,11},{9,10},{10,... | collective-permute-start | bytes 196616 | tf_op jit(solution)/shard_map/ppermute | solution.py:33
  93.6 8.9 %collective-permute-start.34 = (f32[64,256]{1,0:T(8,128)S(1)}, f32[64,256]{1,0:T(8,128)S(1)}, u32[]{:S(2)}, u32[]{:S(2)}) collective-permute-start(f32[64,256]{1,0:T(8,128)S(1)} %fusion.5), channel_id=1, source_target_pairs={{0,2},{1,3},{2,0},{3,1},{4,6},{5,7},{6,4},{7,5},{8,10},{9,11},{10,... | collective-permute-start | bytes 196616 | tf_op jit(solution)/shard_map/ppermute | solution.py:33
  93.6 5.8 %collective-permute-start.33 = (f32[64,256]{1,0:T(8,128)S(1)}, f32[64,256]{1,0:T(8,128)S(1)}, u32[]{:S(2)}, u32[]{:S(2)}) collective-permute-start(f32[64,256]{1,0:T(8,128)S(1)} %fusion.5), channel_id=1, source_target_pairs={{0,1},{1,0},{2,3},{3,2},{4,5},{5,4},{6,7},{7,6},{8,9},{9,8},{10,11... | collective-permute-start | bytes 196616 | tf_op jit(solution)/shard_map/ppermute | solution.py:33
  97.3 10.3 %collective-permute-start.41 = (f32[64,256]{1,0:T(8,128)S(1)}, f32[64,256]{1,0:T(8,128)S(1)}, u32[]{:S(2)}, u32[]{:S(2)}) collective-permute-start(f32[64,256]{1,0:T(8,128)S(1)} %fusion.2), channel_id=1, source_target_pairs={{0,3},{1,2},{2,1},{3,0},{4,7},{5,6},{6,5},{7,4},{8,11},{9,10},{10,... | collective-permute-start | bytes 196616 | tf_op jit(solution)/shard_map/ppermute | solution.py:33
  99.2 8.7 %collective-permute-start.40 = (f32[64,256]{1,0:T(8,128)S(1)}, f32[64,256]{1,0:T(8,128)S(1)}, u32[]{:S(2)}, u32[]{:S(2)}) collective-permute-start(f32[64,256]{1,0:T(8,128)S(1)} %fusion.2), channel_id=1, source_target_pairs={{0,2},{1,3},{2,0},{3,1},{4,6},{5,7},{6,4},{7,5},{8,10},{9,11},{10,... | collective-permute-start | bytes 196616 | tf_op jit(solution)/shard_map/ppermute | solution.py:33
  99.3 5.4 %collective-permute-start.39 = (f32[64,256]{1,0:T(8,128)S(1)}, f32[64,256]{1,0:T(8,128)S(1)}, u32[]{:S(2)}, u32[]{:S(2)}) collective-permute-start(f32[64,256]{1,0:T(8,128)S(1)} %fusion.2), channel_id=1, source_target_pairs={{0,1},{1,0},{2,3},{3,2},{4,5},{5,4},{6,7},{7,6},{8,9},{9,8},{10,11... | collective-permute-start | bytes 196616 | tf_op jit(solution)/shard_map/ppermute | solution.py:33
  102.8 9.9 %collective-permute-start.44 = (f32[64,256]{1,0:T(8,128)S(1)}, f32[64,256]{1,0:T(8,128)S(1)}, u32[]{:S(2)}, u32[]{:S(2)}) collective-permute-start(f32[64,256]{1,0:T(8,128)S(1)} %get-tuple-element.57.refs_6_), channel_id=1, source_target_pairs={{0,3},{1,2},{2,1},{3,0},{4,7},{5,6},{6,5},{7,4},{8,11},{9,10},{10,... | collective-permute-start | bytes 196616 | tf_op jit(solution)/shard_map/ppermute | solution.py:33
  104.8 7.9 %collective-permute-start.43 = (f32[64,256]{1,0:T(8,128)S(1)}, f32[64,256]{1,0:T(8,128)S(1)}, u32[]{:S(2)}, u32[]{:S(2)}) collective-permute-start(f32[64,256]{1,0:T(8,128)S(1)} %get-tuple-element.57.refs_6_), channel_id=1, source_target_pairs={{0,2},{1,3},{2,0},{3,1},{4,6},{5,7},{6,4},{7,5},{8,10},{9,11},{10,... | collective-permute-start | bytes 196616 | tf_op jit(solution)/shard_map/ppermute | solution.py:33
  104.8 5.4 %collective-permute-start.42 = (f32[64,256]{1,0:T(8,128)S(1)}, f32[64,256]{1,0:T(8,128)S(1)}, u32[]{:S(2)}, u32[]{:S(2)}) collective-permute-start(f32[64,256]{1,0:T(8,128)S(1)} %get-tuple-element.57.refs_6_), channel_id=1, source_target_pairs={{0,1},{1,0},{2,3},{3,2},{4,5},{5,4},{6,7},{7,6},{8,9},{9,8},{10,11... | collective-permute-start | bytes 196616 | tf_op jit(solution)/shard_map/ppermute | solution.py:33
  108.2 7.5 %collective-permute-start.47 = (f32[64,256]{1,0:T(8,128)S(1)}, f32[64,256]{1,0:T(8,128)S(1)}, u32[]{:S(2)}, u32[]{:S(2)}) collective-permute-start(f32[64,256]{1,0:T(8,128)S(1)} %get-tuple-element.65.refs_7_), channel_id=1, source_target_pairs={{0,3},{1,2},{2,1},{3,0},{4,7},{5,6},{6,5},{7,4},{8,11},{9,10},{10,... | collective-permute-start | bytes 196616 | tf_op jit(solution)/shard_map/ppermute | solution.py:33
  110.2 5.6 %collective-permute-start.46 = (f32[64,256]{1,0:T(8,128)S(1)}, f32[64,256]{1,0:T(8,128)S(1)}, u32[]{:S(2)}, u32[]{:S(2)}) collective-permute-start(f32[64,256]{1,0:T(8,128)S(1)} %get-tuple-element.65.refs_7_), channel_id=1, source_target_pairs={{0,2},{1,3},{2,0},{3,1},{4,6},{5,7},{6,4},{7,5},{8,10},{9,11},{10,... | collective-permute-start | bytes 196616 | tf_op jit(solution)/shard_map/ppermute | solution.py:33
  110.2 4.9 %collective-permute-start.45 = (f32[64,256]{1,0:T(8,128)S(1)}, f32[64,256]{1,0:T(8,128)S(1)}, u32[]{:S(2)}, u32[]{:S(2)}) collective-permute-start(f32[64,256]{1,0:T(8,128)S(1)} %get-tuple-element.65.refs_7_), channel_id=1, source_target_pairs={{0,1},{1,0},{2,3},{3,2},{4,5},{5,4},{6,7},{7,6},{8,9},{9,8},{10,11... | collective-permute-start | bytes 196616 | tf_op jit(solution)/shard_map/ppermute | solution.py:33
  117.3 1.4 collective-permute-start.48
  118.8 4.6 %collective-permute-start.49 = (f32[2,16,512]{2,1,0:T(8,128)S(1)}, f32[2,16,512]{2,1,0:T(8,128)S(1)}, u32[]{:S(2)}, u32[]{:S(2)}) collective-permute-start(f32[2,16,512]{2,1,0:T(8,128)S(1)} %get-tuple-element.37), channel_id=1, source_target_pairs={{0,8},{4,12},{8,0},{12,4},{16,24},{20,28},{24,16},{28,20},{1,9},{5... | collective-permute-start | bytes 196616 | tf_op jit(solution)/shard_map/ppermute | solution.py:71
  120.3 4.3 %collective-permute-start.50 = (f32[2,16,512]{2,1,0:T(8,128)S(1)}, f32[2,16,512]{2,1,0:T(8,128)S(1)}, u32[]{:S(2)}, u32[]{:S(2)}) collective-permute-start(f32[2,16,512]{2,1,0:T(8,128)S(1)} %get-tuple-element.38), channel_id=1, source_target_pairs={{0,16},{4,20},{8,24},{12,28},{16,0},{20,4},{24,8},{28,12},{1,17},{... | collective-permute-start | bytes 196616 | tf_op jit(solution)/shard_map/ppermute | solution.py:71
  121.8 5.2 %collective-permute-start.51 = (f32[2,16,512]{2,1,0:T(8,128)S(1)}, f32[2,16,512]{2,1,0:T(8,128)S(1)}, u32[]{:S(2)}, u32[]{:S(2)}) collective-permute-start(f32[2,16,512]{2,1,0:T(8,128)S(1)} %get-tuple-element.39), channel_id=1, source_target_pairs={{0,24},{4,28},{8,16},{12,20},{16,8},{20,12},{24,0},{28,4},{1,25},{... | collective-permute-start | bytes 196616 | tf_op jit(solution)/shard_map/ppermute | solution.py:71
  128.4 5.3 %collective-permute-start.52 = (f32[16,1280]{1,0:T(8,128)S(1)}, f32[16,1280]{1,0:T(8,128)S(1)}, u32[]{:S(2)}, u32[]{:S(2)}) collective-permute-start(f32[16,1280]{1,0:T(8,128)S(1)} %get-tuple-element.41), channel_id=1, source_target_pairs={{0,1},{1,0},{2,3},{3,2},{4,5},{5,4},{6,7},{7,6},{8,9},{9,8},{10,11... | collective-permute-start | bytes 245768 | tf_op jit(solution)/shard_map/ppermute | solution.py:33
  129.7 7.8 %collective-permute-start.53 = (f32[16,1280]{1,0:T(8,128)S(1)}, f32[16,1280]{1,0:T(8,128)S(1)}, u32[]{:S(2)}, u32[]{:S(2)}) collective-permute-start(f32[16,1280]{1,0:T(8,128)S(1)} %get-tuple-element.42), channel_id=1, source_target_pairs={{0,2},{1,3},{2,0},{3,1},{4,6},{5,7},{6,4},{7,5},{8,10},{9,11},{10,... | collective-permute-start | bytes 245768 | tf_op jit(solution)/shard_map/ppermute | solution.py:33
  131.0 6.6 %collective-permute-start.54 = (f32[16,1280]{1,0:T(8,128)S(1)}, f32[16,1280]{1,0:T(8,128)S(1)}, u32[]{:S(2)}, u32[]{:S(2)}) collective-permute-start(f32[16,1280]{1,0:T(8,128)S(1)} %get-tuple-element.43), channel_id=1, source_target_pairs={{0,3},{1,2},{2,1},{3,0},{4,7},{5,6},{6,5},{7,4},{8,11},{9,10},{10,... | collective-permute-start | bytes 245768 | tf_op jit(solution)/shard_map/ppermute | solution.py:33
  138.0 5.6 %collective-permute-start.57 = (f32[16,256]{1,0:T(8,128)S(1)}, f32[16,256]{1,0:T(8,128)S(1)}, u32[]{:S(2)}, u32[]{:S(2)}) collective-permute-start(f32[16,256]{1,0:T(8,128)S(1)} %get-tuple-element.46.refs_0_), channel_id=1, source_target_pairs={{0,3},{1,2},{2,1},{3,0},{4,7},{5,6},{6,5},{7,4},{8,11},{9,10},{10,... | collective-permute-start | bytes 49160 | tf_op jit(solution)/shard_map/ppermute | solution.py:33
  139.9 5.0 %collective-permute-start.56 = (f32[16,256]{1,0:T(8,128)S(1)}, f32[16,256]{1,0:T(8,128)S(1)}, u32[]{:S(2)}, u32[]{:S(2)}) collective-permute-start(f32[16,256]{1,0:T(8,128)S(1)} %get-tuple-element.46.refs_0_), channel_id=1, source_target_pairs={{0,2},{1,3},{2,0},{3,1},{4,6},{5,7},{6,4},{7,5},{8,10},{9,11},{10,... | collective-permute-start | bytes 49160 | tf_op jit(solution)/shard_map/ppermute | solution.py:33
  141.0 3.9 %collective-permute-start.55 = (f32[16,256]{1,0:T(8,128)S(1)}, f32[16,256]{1,0:T(8,128)S(1)}, u32[]{:S(2)}, u32[]{:S(2)}) collective-permute-start(f32[16,256]{1,0:T(8,128)S(1)} %get-tuple-element.46.refs_0_), channel_id=1, source_target_pairs={{0,1},{1,0},{2,3},{3,2},{4,5},{5,4},{6,7},{7,6},{8,9},{9,8},{10,11... | collective-permute-start | bytes 49160 | tf_op jit(solution)/shard_map/ppermute | solution.py:33
  145.4 5.6 %collective-permute-start.60 = (f32[16,256]{1,0:T(8,128)S(1)}, f32[16,256]{1,0:T(8,128)S(1)}, u32[]{:S(2)}, u32[]{:S(2)}) collective-permute-start(f32[16,256]{1,0:T(8,128)S(1)} %shard_map.122.refs_0_), channel_id=1, source_target_pairs={{0,3},{1,2},{2,1},{3,0},{4,7},{5,6},{6,5},{7,4},{8,11},{9,10},{10,... | collective-permute-start | bytes 49160 | tf_op jit(solution)/shard_map/ppermute | solution.py:33
  147.4 4.7 %collective-permute-start.59 = (f32[16,256]{1,0:T(8,128)S(1)}, f32[16,256]{1,0:T(8,128)S(1)}, u32[]{:S(2)}, u32[]{:S(2)}) collective-permute-start(f32[16,256]{1,0:T(8,128)S(1)} %shard_map.122.refs_0_), channel_id=1, source_target_pairs={{0,2},{1,3},{2,0},{3,1},{4,6},{5,7},{6,4},{7,5},{8,10},{9,11},{10,... | collective-permute-start | bytes 49160 | tf_op jit(solution)/shard_map/ppermute | solution.py:33
  148.2 3.9 %collective-permute-start.58 = (f32[16,256]{1,0:T(8,128)S(1)}, f32[16,256]{1,0:T(8,128)S(1)}, u32[]{:S(2)}, u32[]{:S(2)}) collective-permute-start(f32[16,256]{1,0:T(8,128)S(1)} %shard_map.122.refs_0_), channel_id=1, source_target_pairs={{0,1},{1,0},{2,3},{3,2},{4,5},{5,4},{6,7},{7,6},{8,9},{9,8},{10,11... | collective-permute-start | bytes 49160 | tf_op jit(solution)/shard_map/ppermute | solution.py:33
  (10 other events, 159.8 us)

commit v11 on v10

--- a/solution.py
+++ b/solution.py
@@ -33,15 +33,30 @@
     return lax.ppermute(value, axis, pairs)
 
 
-def gather_rows(value):
+def gather_rows(value, stream=0):
     members = lax.axis_size("grp")
     me = lax.axis_index("grp")
     rows = value.shape[1]
     pieces = [(me * rows, value)]
-    for distance in range(1, members):
+    distances = list(range(members - 1, 0, -1))
+    if stream % 2:
+        distances[:2] = distances[1::-1]
+    for distance in distances:
         owner = partner(me, distance, members)
         pieces.append((owner * rows, send(value, "grp", distance)))
     return pieces
+
+
+def gather_small(value):
+    members = lax.axis_size("grp")
+    if members & (members - 1):
+        return [value] + [send(value, "grp", d) for d in range(1, members)]
+    held = value[None]
+    distance = 1
+    while distance < members:
+        held = jnp.concatenate([held, send(held, "grp", distance)], axis=0)
+        distance *= 2
+    return [held]
 
 
 def assemble(pieces, order):
@@ -75,7 +90,7 @@
 SMEM = pl.BlockSpec(memory_space=pltpu.SMEM)
 
 
-def local_kernel(body, outs, operands, specs=None, flops=0, scratch=()):
+def local_kernel(body, outs, operands, specs=None, flops=0, scratch=(), limit=None):
     size = sum(o.size * o.dtype.itemsize for o in list(outs) + list(operands))
     return pl.pallas_call(
         body,
@@ -84,7 +99,7 @@
         out_specs=[VMEM] * len(outs),
         scratch_shapes=list(scratch),
         cost_estimate=pl.CostEstimate(flops=flops, bytes_accessed=size, transcendentals=0),
-        compiler_params=pltpu.CompilerParams(vmem_limit_bytes=2 * size + 2**21),
+        compiler_params=pltpu.CompilerParams(vmem_limit_bytes=limit or 2 * size + 2**21),
     )(*operands)
 
 
@@ -194,16 +209,25 @@
     rows, count = rhs.shape[2:]
     depth = count // streams
 
-    def body(rhs_ref, *outs):
-        for index in range(first, last):
-            wide = jnp.transpose(rhs_ref[0, index - first])
+    def body(rhs_ref, *refs):
+        outs, (held, sem) = refs[:-2], refs[-2:]
+        copy = pltpu.make_async_copy(rhs_ref.at[0, first:last], held, sem)
+        copy.start()
+        copy.wait()
+        for index in range(last - first):
+            wide = jnp.transpose(held[index])
             for i in range(streams):
-                outs[(index - first) * streams + i][...] = wide[i * depth : (i + 1) * depth]
+                outs[index * streams + i][...] = wide[i * depth : (i + 1) * depth]
 
     return local_kernel(
         body,
         [float_array(depth, rows)] * (streams * (last - first)),
-        [rhs[:, first:last]],
+        [rhs],
+        [pl.BlockSpec(memory_space=pl.ANY)],
+        scratch=[
+            pltpu.VMEM((last - first, rows, count), jnp.float32),
+            pltpu.SemaphoreType.DMA(()),
+        ],
     )
 
 
@@ -213,19 +237,20 @@
     depth, rows = flat[0].shape
 
     def body(*refs):
-        out = refs[-1]
+        out, tie = refs[-2:]
         for index in range(len(solved)):
             wide = jnp.concatenate(
                 [refs[index * streams + i][...] for i in range(streams)], axis=0
             )
             out[0, index] = jnp.transpose(wide)
-
-    return local_kernel(
-        body,
-        [float_array(1, len(solved), rows, depth * streams)],
+        tie[...] = jnp.zeros(tie.shape, jnp.float32)
+
+    return local_kernel(
+        body,
+        [float_array(1, len(solved), rows, depth * streams), float_array(8, 128)],
         [*flat, after],
         [VMEM] * len(flat) + [pl.BlockSpec(memory_space=pl.ANY)],
-    )[0]
+    )
 
 
 def leaf_exchange(packed):
@@ -339,26 +364,71 @@
     )
 
 
+def put_in_order(held, whole):
+    me = lax.axis_index("grp")
+    members = len(held)
+    width = held[0].shape[1]
+    for j in range(members):
+        value = jnp.zeros(held[0].shape, jnp.float32)
+        for distance in range(members):
+            owner = partner(me, distance, members) if distance else me
+            value = jnp.where(owner == j, held[distance], value)
+        whole[:, j * width : (j + 1) * width] = value
+
+
+def apply_first(value, stream, factor):
+    members = lax.axis_size("grp")
+    depth, width = value.shape
+    rows, order = factor.shape[2:]
+    order_of = list(range(members - 1, 0, -1))
+    if stream % 2:
+        order_of[:2] = order_of[1::-1]
+    held = {0: value}
+    for distance in order_of:
+        held[distance] = send(value, "grp", distance)
+
+    def body(*refs):
+        factor_ref, out, whole, matrix, sem = refs[members:]
+        copy = pltpu.make_async_copy(factor_ref.at[0, 0], matrix, sem)
+        copy.start()
+        put_in_order([refs[d][...] for d in range(members)], whole)
+        copy.wait()
+        top, rest = high_low(matrix[...])
+        out[...] = split_product(whole[...], top, rest)
+
+    return local_kernel(
+        body,
+        [float_array(depth, rows)],
+        [held[d] for d in range(members)] + [factor],
+        [VMEM] * members + [pl.BlockSpec(memory_space=pl.ANY)],
+        flops=6 * depth * rows * order,
+        scratch=[
+            pltpu.VMEM((depth, order), jnp.float32),
+            pltpu.VMEM((rows, order), jnp.float32),
+            pltpu.SemaphoreType.DMA(()),
+        ],
+        limit=2**24,
+    )[0]
+
+
 def apply_split(pieces, top, rest, index, base=None, begin=0):
     members = lax.axis_size("grp")
-    part, width = pieces[0].shape
+    part, width = pieces[0].shape[-2:]
     rows, order = top.shape[1:]
     extra = [] if base is None else [base]
-
-    def body(*refs):
-        held = refs[:members]
-        top_ref, rest_ref = refs[members : members + 2]
+    count = len(pieces)
+
+    def body(*refs):
+        top_ref, rest_ref = refs[count : count + 2]
         out, whole = refs[-2:]
-        me = lax.axis_index("grp")
-        for j in range(members):
-            value = jnp.zeros((part, width), jnp.float32)
-            for distance in range(members):
-                owner = partner(me, distance, members) if distance else me
-                value = jnp.where(owner == j, held[distance][...], value)
-            whole[:, j * width : (j + 1) * width] = value
+        if count == 1:
+            held = [refs[0][d] for d in range(members)]
+        else:
+            held = [refs[d][...] for d in range(members)]
+        put_in_order(held, whole)
         result = split_product(whole[...], top_ref[index], rest_ref[index])
         if extra:
-            result = refs[members + 2][:, begin : begin + rows] - result
+            result = refs[count + 2][:, begin : begin + rows] - result
         out[...] = result
 
     return local_kernel(
@@ -396,14 +466,13 @@
     for current in range(supernodes):
         owned = []
         for residual in residuals:
-            pieces = gather_rows(residual)
             if current:
+                pieces = gather_rows(residual, len(owned))
                 owned.append(apply_pieces(diag_inv_local, current, pieces))
             else:
-                whole = assemble(pieces, order)
-                owned.append(contract_last(whole, diag_inv_local[0, current]))
+                owned.append(apply_first(residual, len(owned), diag_inv_local))
         solved.append(owned)
-        held = [gather_rows(value) for value in owned]
+        held = [gather_rows(value, i) for i, value in enumerate(owned)]
         gathered.append([assemble(pieces, order) for pieces in held])
         if current + 1 < supernodes:
             residuals = [
@@ -415,9 +484,9 @@
     done = [tile_terms(values, tiles[0, 0], tile_source) for values in by_stream[:-1]]
     packed = pack_terms(done, by_stream[-1], tiles[0, 0], tile_source, tile_block, tile_count)
     received = leaf_exchange(packed)
-    solution_local = turn_back(solved, packed[0])
+    solution_local, tie = turn_back(solved, packed[0])
     shares = share_out(
-        received, jnp.swapaxes(rhs_anc, 1, 2), order, slots, tile_rows, solution_local
+        received, jnp.swapaxes(rhs_anc, 1, 2), order, slots, tile_rows, tie
     )
     payloads = [shares[0]] + [send(shares[d], "grp", d) for d in range(1, members)]
     inverse_top, inverse_rest, below_top, below_rest = split_factors(
@@ -426,11 +495,11 @@
     solution, left = solve_first(payloads, inverse_top, inverse_rest)
     solutions = [solution]
     for ancestor in range(1, rhs_anc.shape[0]):
-        pieces = [piece for _, piece in gather_rows(solutions[-1])]
+        pieces = gather_small(solutions[-1])
         residual = apply_split(
             pieces, below_top, below_rest, ancestor - 1, left, (ancestor - 1) * rows
         )
-        pieces = [piece for _, piece in gather_rows(residual)]
+        pieces = gather_small(residual)
         solutions.append(apply_split(pieces, inverse_top, inverse_rest, ancestor))
     solutions = jnp.swapaxes(jnp.stack(solutions), 1, 2)
     return (solution_local, solutions)

time: 154 us -> 156 us (1.013)
  waiting for transfers between devices: 30.9 us -> 42.7 us
  starting transfers between devices: 86.2 us -> 77.7 us
  matrix products: 17.3 us -> 13.6 us
  Pallas kernels: 6.79 us -> 9.45 us
    ppermute x57 -> x55, waiting for transfers between devices: 25.8 us -> 38.4 us  [send(): return lax.ppermute(value, axis, pairs)]
    ppermute x57 -> x55, starting transfers between devices: 82.6 us -> 73 us  [send(): return lax.ppermute(value, axis, pairs)]
    unnamed x26 -> x46, local copies, waits for them, and re-layouts: 2.34 us -> 8.2 us
    dynamic_update_slice x32 -> x26, local copies, waits for them, and re-layouts: 4.53 us -> 0.29 us  [assemble(): whole = lax.dynamic_update_slice_in_dim(whole, piece, offset, 1)]
    dot_general x50 -> x48, matrix products: 17.3 us -> 13.6 us  [contract_last(): lax.dot_general(left, right, (((left.ndim - 1,), (right.ndim - 1,)), ((),...]
    pallas_call x11 -> x13, Pallas kernels: 6.79 us -> 9.45 us  [local_kernel(): pl.pallas_call(body, out_shape=list(outs), in_specs=specs or [VMEM] * len...]
    slice x2 -> x0, local copies, waits for them, and re-layouts: 2.09 us -> none  [turn(): rhs[:, first:last]]
  transfers between devices with their start and end apart: 61 -> 59, of which waited for: 19 -> 22; matrix products, arithmetic and copies ran while one was open for 15% -> 9% of each run, Pallas kernels for 2% -> 4%
where the time goes in v11:
time: 156 us; the launch traced here: 155 us
  starting transfers between devices  77.7 us (50%)
  waiting for transfers between devices  42.7 us (27%)
  matrix products  13.6 us (9%)
  Pallas kernels  9.45 us (6%)
  local copies, waits for them, and re-layouts  8.65 us (6%)
  between operations  2.54 us (2%)
    ppermute x55, starting transfers between devices, send(): return lax.ppermute(value, axis, pairs)  73 us
    ppermute x55, waiting for transfers between devices, send(): return lax.ppermute(value, axis, pairs)  38.4 us
    dot_general x48, matrix products, contract_last(): lax.dot_general(left, right, (((left.ndim - 1,), (right.ndim - 1,)), ((),...  13.6 us
    pallas_call x13, Pallas kernels, local_kernel(): pl.pallas_call(body, out_shape=list(outs), in_specs=specs or [VMEM] * len...  9.45 us
    unnamed x46, local copies, waits for them, and re-layouts  8.2 us
    ppermute x3, starting transfers between devices, swap(): return lax.ppermute(value, axis, pairs)  4.7 us
  transfers between devices with their start and end apart: 59, of which 22 were waited for; matrix products, arithmetic and copies ran while one was open for 9% of the time, Pallas kernels for 4%

profile of v11, /device:TPU:0, one launch (start us, length us, event | category | flops | bytes accessed | tf_op | source)
XLA Modules:
  0.0 155.4 jit_solution(12849212985799369325)
XLA Ops:
  0.7 1.2 copy-done.5
  2.1 5.1 %collective-permute-start.2 = (f32[64,256]{1,0:T(8,128)S(1)}, f32[64,256]{1,0:T(8,128)S(1)}, u32[]{:S(2)}, u32[]{:S(2)}) collective-permute-start(f32[64,256]{1,0:T(8,128)S(1)} %get-tuple-element.28.refs_0_), channel_id=1, source_target_pairs={{0,3},{1,2},{2,1},{3,0},{4,7},{5,6},{6,5},{7,4},{8,11},{9,10},{10,... | collective-permute-start | bytes 196616 | tf_op jit(solution)/shard_map/ppermute | solution.py:33
  7.8 3.7 %collective-permute-start.5 = (f32[64,256]{1,0:T(8,128)S(1)}, f32[64,256]{1,0:T(8,128)S(1)}, u32[]{:S(2)}, u32[]{:S(2)}) collective-permute-start(f32[64,256]{1,0:T(8,128)S(1)} %get-tuple-element.29.refs_0_), channel_id=1, source_target_pairs={{0,3},{1,2},{2,1},{3,0},{4,7},{5,6},{6,5},{7,4},{8,11},{9,10},{10,... | collective-permute-start | bytes 196616 | tf_op jit(solution)/shard_map/ppermute | solution.py:33
  11.6 0.8 collective-permute-start.3
  12.4 1.0 copy-done.6
  18.3 2.2 %copy-done.1 = f32[1,4,256,1024]{3,2,1,0:T(8,128)S(1)} copy-done((f32[1,4,256,1024]{3,2,1,0:T(8,128)S(1)}, f32[1,4,256,1024]{3,2,1,0:T(8,128)}, u32[]{:S(2)}) %copy-start.1) | copy-done | bytes 4194328
  20.4 1.8 %shard_map.114.refs_0_ = f32[64,256]{1,0:T(8,128)S(1)} custom-call(f32[64,256]{1,0:T(8,128)S(1)} %get-tuple-element.28.refs_0_, f32[64,256]{1,0:T(8,128)} %collective-permute-done.refs_1_, f32[64,256]{1,0:T(8,128)} %collective-permute-done.1.refs_2_, f32[64,256]{1,0:T(8,128)S(1)} %collective-permute-done.2.refs_3_, f32[1,4,256,1024]{3,2,1,0:T(8,128)S(1)} %copy-done.1), custom_call_target="tpu_custom_call" | custom-call | flops 100663296 | bytes 4521984 | tf_op jit(solution)/shard_map/pallas_call | solution.py:95
  22.2 1.3 collective-permute-start.8
  23.5 2.9 %collective-permute-start.7 = (f32[64,256]{1,0:T(8,128)S(1)}, f32[64,256]{1,0:T(8,128)S(1)}, u32[]{:S(2)}, u32[]{:S(2)}) collective-permute-start(f32[64,256]{1,0:T(8,128)S(1)} %shard_map.114.refs_0_), channel_id=1, source_target_pairs={{0,2},{1,3},{2,0},{3,1},{4,6},{5,7},{6,4},{7,5},{8,10},{9,11},{10,... | collective-permute-start | bytes 196616 | tf_op jit(solution)/shard_map/ppermute | solution.py:33
  26.7 0.7 shard_map.115.refs_1_
  27.8 3.3 %collective-permute-start.13 = (f32[64,256]{1,0:T(8,128)S(1)}, f32[64,256]{1,0:T(8,128)S(1)}, u32[]{:S(2)}, u32[]{:S(2)}) collective-permute-start(f32[64,256]{1,0:T(8,128)S(1)} %shard_map.115.refs_1_), channel_id=1, source_target_pairs={{0,3},{1,2},{2,1},{3,0},{4,7},{5,6},{6,5},{7,4},{8,11},{9,10},{10,... | collective-permute-start | bytes 196616 | tf_op jit(solution)/shard_map/ppermute | solution.py:33
  33.9 1.5 collective-permute-start.11
  35.4 1.5 collective-permute-start.10
  36.8 1.5 collective-permute-start.9
  40.4 2.4 %collective-permute-start.16 = (f32[64,256]{1,0:T(8,128)S(1)}, f32[64,256]{1,0:T(8,128)S(1)}, u32[]{:S(2)}, u32[]{:S(2)}) collective-permute-start(f32[64,256]{1,0:T(8,128)S(1)} %fusion.15), channel_id=1, source_target_pairs={{0,3},{1,2},{2,1},{3,0},{4,7},{5,6},{6,5},{7,4},{8,11},{9,10},{10,... | collective-permute-start | bytes 196616 | tf_op jit(solution)/shard_map/ppermute | solution.py:33
  43.3 1.6 %collective-permute-start.15 = (f32[64,256]{1,0:T(8,128)S(1)}, f32[64,256]{1,0:T(8,128)S(1)}, u32[]{:S(2)}, u32[]{:S(2)}) collective-permute-start(f32[64,256]{1,0:T(8,128)S(1)} %fusion.15), channel_id=1, source_target_pairs={{0,2},{1,3},{2,0},{3,1},{4,6},{5,7},{6,4},{7,5},{8,10},{9,11},{10,... | collective-permute-start | bytes 196616 | tf_op jit(solution)/shard_map/ppermute | solution.py:33
  46.4 2.3 %collective-permute-start.19 = (f32[64,256]{1,0:T(8,128)S(1)}, f32[64,256]{1,0:T(8,128)S(1)}, u32[]{:S(2)}, u32[]{:S(2)}) collective-permute-start(f32[64,256]{1,0:T(8,128)S(1)} %get-tuple-element.55.refs_2_), channel_id=1, source_target_pairs={{0,2},{1,3},{2,0},{3,1},{4,6},{5,7},{6,4},{7,5},{8,10},{9,11},{10,... | collective-permute-start | bytes 196616 | tf_op jit(solution)/shard_map/ppermute | solution.py:33
  48.8 2.1 %collective-permute-done.15 = f32[64,256]{1,0:T(8,128)S(1)} collective-permute-done((f32[64,256]{1,0:T(8,128)S(1)}, f32[64,256]{1,0:T(8,128)S(1)}, u32[]{:S(2)}, u32[]{:S(2)}) %collective-permute-start.15) | collective-permute-done | bytes 65568 | tf_op jit(solution)/shard_map/ppermute | solution.py:33
  50.8 1.5 collective-permute-start.18
  53.6 2.4 %collective-permute-start.25 = (f32[64,256]{1,0:T(8,128)S(1)}, f32[64,256]{1,0:T(8,128)S(1)}, u32[]{:S(2)}, u32[]{:S(2)}) collective-permute-start(f32[64,256]{1,0:T(8,128)S(1)} %get-tuple-element.61.refs_3_), channel_id=1, source_target_pairs={{0,3},{1,2},{2,1},{3,0},{4,7},{5,6},{6,5},{7,4},{8,11},{9,10},{10,... | collective-permute-start | bytes 196616 | tf_op jit(solution)/shard_map/ppermute | solution.py:33
  56.0 1.4 collective-permute-done.18
  58.9 1.5 collective-permute-start.23
  60.3 1.4 collective-permute-start.22
  61.7 1.9 %collective-permute-done.24 = f32[64,256]{1,0:T(8,128)S(1)} collective-permute-done((f32[64,256]{1,0:T(8,128)S(1)}, f32[64,256]{1,0:T(8,128)S(1)}, u32[]{:S(2)}, u32[]{:S(2)}) %collective-permute-start.24) | collective-permute-done | bytes 65568 | tf_op jit(solution)/shard_map/ppermute | solution.py:33
  63.6 1.9 %collective-permute-start.21 = (f32[64,256]{1,0:T(8,128)S(1)}, f32[64,256]{1,0:T(8,128)S(1)}, u32[]{:S(2)}, u32[]{:S(2)}) collective-permute-start(f32[64,256]{1,0:T(8,128)S(1)} %fusion.11), channel_id=1, source_target_pairs={{0,3},{1,2},{2,1},{3,0},{4,7},{5,6},{6,5},{7,4},{8,11},{9,10},{10,... | collective-permute-start | bytes 196616 | tf_op jit(solution)/shard_map/ppermute | solution.py:33
  66.8 2.0 %collective-permute-start.28 = (f32[64,256]{1,0:T(8,128)S(1)}, f32[64,256]{1,0:T(8,128)S(1)}, u32[]{:S(2)}, u32[]{:S(2)}) collective-permute-start(f32[64,256]{1,0:T(8,128)S(1)} %fusion.8), channel_id=1, source_target_pairs={{0,3},{1,2},{2,1},{3,0},{4,7},{5,6},{6,5},{7,4},{8,11},{9,10},{10,... | collective-permute-start | bytes 196616 | tf_op jit(solution)/shard_map/ppermute | solution.py:33
  68.9 1.1 collective-permute-done.21
  71.7 2.3 %collective-permute-start.32 = (f32[64,256]{1,0:T(8,128)S(1)}, f32[64,256]{1,0:T(8,128)S(1)}, u32[]{:S(2)}, u32[]{:S(2)}) collective-permute-start(f32[64,256]{1,0:T(8,128)S(1)} %get-tuple-element.57.refs_4_), channel_id=1, source_target_pairs={{0,1},{1,0},{2,3},{3,2},{4,5},{5,4},{6,7},{7,6},{8,9},{9,8},{10,11... | collective-permute-start | bytes 196616 | tf_op jit(solution)/shard_map/ppermute | solution.py:33
  74.3 3.3 %collective-permute-done.27 = f32[64,256]{1,0:T(8,128)S(1)} collective-permute-done((f32[64,256]{1,0:T(8,128)S(1)}, f32[64,256]{1,0:T(8,128)S(1)}, u32[]{:S(2)}, u32[]{:S(2)}) %collective-permute-start.27) | collective-permute-done | bytes 65568 | tf_op jit(solution)/shard_map/ppermute | solution.py:33
  77.6 2.1 %collective-permute-start.30 = (f32[64,256]{1,0:T(8,128)S(1)}, f32[64,256]{1,0:T(8,128)S(1)}, u32[]{:S(2)}, u32[]{:S(2)}) collective-permute-start(f32[64,256]{1,0:T(8,128)S(1)} %get-tuple-element.57.refs_4_), channel_id=1, source_target_pairs={{0,3},{1,2},{2,1},{3,0},{4,7},{5,6},{6,5},{7,4},{8,11},{9,10},{10,... | collective-permute-start | bytes 196616 | tf_op jit(solution)/shard_map/ppermute | solution.py:33
  81.0 1.8 %collective-permute-start.37 = (f32[64,256]{1,0:T(8,128)S(1)}, f32[64,256]{1,0:T(8,128)S(1)}, u32[]{:S(2)}, u32[]{:S(2)}) collective-permute-start(f32[64,256]{1,0:T(8,128)S(1)} %get-tuple-element.63.refs_5_), channel_id=1, source_target_pairs={{0,3},{1,2},{2,1},{3,0},{4,7},{5,6},{6,5},{7,4},{8,11},{9,10},{10,... | collective-permute-start | bytes 196616 | tf_op jit(solution)/shard_map/ppermute | solution.py:33
  82.8 0.9 collective-permute-done.30
  83.7 0.8 collective-permute-start.36
  85.7 1.9 %collective-permute-start.35 = (f32[64,256]{1,0:T(8,128)S(1)}, f32[64,256]{1,0:T(8,128)S(1)}, u32[]{:S(2)}, u32[]{:S(2)}) collective-permute-start(f32[64,256]{1,0:T(8,128)S(1)} %fusion.5), channel_id=1, source_target_pairs={{0,1},{1,0},{2,3},{3,2},{4,5},{5,4},{6,7},{7,6},{8,9},{9,8},{10,11... | collective-permute-start | bytes 196616 | tf_op jit(solution)/shard_map/ppermute | solution.py:33
  88.1 3.4 %collective-permute-done.36 = f32[64,256]{1,0:T(8,128)S(1)} collective-permute-done((f32[64,256]{1,0:T(8,128)S(1)}, f32[64,256]{1,0:T(8,128)S(1)}, u32[]{:S(2)}, u32[]{:S(2)}) %collective-permute-start.36) | collective-permute-done | bytes 65568 | tf_op jit(solution)/shard_map/ppermute | solution.py:33
  91.5 1.6 %collective-permute-start.33 = (f32[64,256]{1,0:T(8,128)S(1)}, f32[64,256]{1,0:T(8,128)S(1)}, u32[]{:S(2)}, u32[]{:S(2)}) collective-permute-start(f32[64,256]{1,0:T(8,128)S(1)} %fusion.5), channel_id=1, source_target_pairs={{0,3},{1,2},{2,1},{3,0},{4,7},{5,6},{6,5},{7,4},{8,11},{9,10},{10,... | collective-permute-start | bytes 196616 | tf_op jit(solution)/shard_map/ppermute | solution.py:33
  94.4 2.3 %collective-permute-start.40 = (f32[64,256]{1,0:T(8,128)S(1)}, f32[64,256]{1,0:T(8,128)S(1)}, u32[]{:S(2)}, u32[]{:S(2)}) collective-permute-start(f32[64,256]{1,0:T(8,128)S(1)} %fusion.2), channel_id=1, source_target_pairs={{0,3},{1,2},{2,1},{3,0},{4,7},{5,6},{6,5},{7,4},{8,11},{9,10},{10,... | collective-permute-start | bytes 196616 | tf_op jit(solution)/shard_map/ppermute | solution.py:33
  96.8 1.4 collective-permute-done.33
  99.1 2.2 %collective-permute-start.44 = (f32[64,256]{1,0:T(8,128)S(1)}, f32[64,256]{1,0:T(8,128)S(1)}, u32[]{:S(2)}, u32[]{:S(2)}) collective-permute-start(f32[64,256]{1,0:T(8,128)S(1)} %get-tuple-element.59.refs_6_), channel_id=1, source_target_pairs={{0,1},{1,0},{2,3},{3,2},{4,5},{5,4},{6,7},{7,6},{8,9},{9,8},{10,11... | collective-permute-start | bytes 196616 | tf_op jit(solution)/shard_map/ppermute | solution.py:33
  101.3 0.9 collective-permute-start.43
  102.1 1.8 %collective-permute-done.39 = f32[64,256]{1,0:T(8,128)S(1)} collective-permute-done((f32[64,256]{1,0:T(8,128)S(1)}, f32[64,256]{1,0:T(8,128)S(1)}, u32[]{:S(2)}, u32[]{:S(2)}) %collective-permute-start.39) | collective-permute-done | bytes 65568 | tf_op jit(solution)/shard_map/ppermute | solution.py:33
  104.0 1.6 %collective-permute-start.42 = (f32[64,256]{1,0:T(8,128)S(1)}, f32[64,256]{1,0:T(8,128)S(1)}, u32[]{:S(2)}, u32[]{:S(2)}) collective-permute-start(f32[64,256]{1,0:T(8,128)S(1)} %get-tuple-element.59.refs_6_), channel_id=1, source_target_pairs={{0,3},{1,2},{2,1},{3,0},{4,7},{5,6},{6,5},{7,4},{8,11},{9,10},{10,... | collective-permute-start | bytes 196616 | tf_op jit(solution)/shard_map/ppermute | solution.py:33
  106.6 2.3 %collective-permute-start.46 = (f32[64,256]{1,0:T(8,128)S(1)}, f32[64,256]{1,0:T(8,128)S(1)}, u32[]{:S(2)}, u32[]{:S(2)}) collective-permute-start(f32[64,256]{1,0:T(8,128)S(1)} %get-tuple-element.65.refs_7_), channel_id=1, source_target_pairs={{0,3},{1,2},{2,1},{3,0},{4,7},{5,6},{6,5},{7,4},{8,11},{9,10},{10,... | collective-permute-start | bytes 196616 | tf_op jit(solution)/shard_map/ppermute | solution.py:33
  108.9 1.2 collective-permute-done.42
  110.2 1.5 shard_map.117.refs_0_
  111.7 3.5 %collective-permute-done.45 = f32[64,256]{1,0:T(8,128)S(1)} collective-permute-done((f32[64,256]{1,0:T(8,128)S(1)}, f32[64,256]{1,0:T(8,128)S(1)}, u32[]{:S(2)}, u32[]{:S(2)}) %collective-permute-start.45) | collective-permute-done | bytes 65568 | tf_op jit(solution)/shard_map/ppermute | solution.py:33
  115.3 1.5 shard_map.118
  116.9 1.3 collective-permute-done.48.refs_1_
  118.3 3.2 %collective-permute-start.49 = (f32[2,16,512]{2,1,0:T(8,128)S(1)}, f32[2,16,512]{2,1,0:T(8,128)S(1)}, u32[]{:S(2)}, u32[]{:S(2)}) collective-permute-start(f32[2,16,512]{2,1,0:T(8,128)S(1)} %get-tuple-element.40), channel_id=1, source_target_pairs={{0,8},{4,12},{8,0},{12,4},{16,24},{20,28},{24,16},{28,20},{1,9},{5... | collective-permute-start | bytes 196616 | tf_op jit(solution)/shard_map/ppermute | solution.py:86
  121.5 1.4 collective-permute-start.51
  123.0 1.0 shard_map.119
  124.0 3.0 %collective-permute-done.50.refs_2_ = f32[2,16,512]{2,1,0:T(8,128)S(1)} collective-permute-done((f32[2,16,512]{2,1,0:T(8,128)S(1)}, f32[2,16,512]{2,1,0:T(8,128)S(1)}, u32[]{:S(2)}, u32[]{:S(2)}) %collective-permute-start.50) | collective-permute-done | bytes 65568 | tf_op jit(solution)/shard_map/ppermute | solution.py:86
  127.5 2.2 %collective-permute-start.53 = (f32[16,1280]{1,0:T(8,128)S(1)}, f32[16,1280]{1,0:T(8,128)S(1)}, u32[]{:S(2)}, u32[]{:S(2)}) collective-permute-start(f32[16,1280]{1,0:T(8,128)S(1)} %get-tuple-element.46), channel_id=1, source_target_pairs={{0,2},{1,3},{2,0},{3,1},{4,6},{5,7},{6,4},{7,5},{8,10},{9,11},{10,... | collective-permute-start | bytes 245768 | tf_op jit(solution)/shard_map/ppermute | solution.py:33
  129.7 2.1 %collective-permute-start.54 = (f32[16,1280]{1,0:T(8,128)S(1)}, f32[16,1280]{1,0:T(8,128)S(1)}, u32[]{:S(2)}, u32[]{:S(2)}) collective-permute-start(f32[16,1280]{1,0:T(8,128)S(1)} %get-tuple-element.47), channel_id=1, source_target_pairs={{0,3},{1,2},{2,1},{3,0},{4,7},{5,6},{6,5},{7,4},{8,11},{9,10},{10,... | collective-permute-start | bytes 245768 | tf_op jit(solution)/shard_map/ppermute | solution.py:33
  132.3 2.8 %collective-permute-done.53.refs_2_ = f32[16,1280]{1,0:T(8,128)S(1)} collective-permute-done((f32[16,1280]{1,0:T(8,128)S(1)}, f32[16,1280]{1,0:T(8,128)S(1)}, u32[]{:S(2)}, u32[]{:S(2)}) %collective-permute-start.53) | collective-permute-done | bytes 81952 | tf_op jit(solution)/shard_map/ppermute | solution.py:33
  135.1 1.0 collective-permute-done.54.refs_3_
  136.6 1.4 collective-permute-start.55
  137.9 2.4 %collective-permute-done.55 = f32[1,16,256]{2,1,0:T(8,128)S(1)} collective-permute-done((f32[1,16,256]{2,1,0:T(8,128)S(1)}, f32[1,16,256]{2,1,0:T(8,128)S(1)}, u32[]{:S(2)}, u32[]{:S(2)}) %collective-permute-start.55) | collective-permute-done | bytes 16416 | tf_op jit(solution)/shard_map/ppermute | solution.py:33
  140.3 1.6 %collective-permute-start.56 = (f32[2,16,256]{2,1,0:T(8,128)S(1)}, f32[2,16,256]{2,1,0:T(8,128)S(1)}, u32[]{:S(2)}, u32[]{:S(2)}) collective-permute-start(f32[2,16,256]{2,1,0:T(8,128)S(1)} %pad_maximum_fusion.2), channel_id=1, source_target_pairs={{0,2},{1,3},{2,0},{3,1},{4,6},{5,7},{6,4},{7,5},{8,10},{9,11},{10,... | collective-permute-start | bytes 98312 | tf_op jit(solution)/shard_map/ppermute | solution.py:33
  142.0 3.2 %collective-permute-done.56 = f32[2,16,256]{2,1,0:T(8,128)S(1)} collective-permute-done((f32[2,16,256]{2,1,0:T(8,128)S(1)}, f32[2,16,256]{2,1,0:T(8,128)S(1)}, u32[]{:S(2)}, u32[]{:S(2)}) %collective-permute-start.56) | collective-permute-done | bytes 32800 | tf_op jit(solution)/shard_map/ppermute | solution.py:33
  145.7 1.4 collective-permute-start.57
  147.0 2.4 %collective-permute-done.57 = f32[1,16,256]{2,1,0:T(8,128)S(1)} collective-permute-done((f32[1,16,256]{2,1,0:T(8,128)S(1)}, f32[1,16,256]{2,1,0:T(8,128)S(1)}, u32[]{:S(2)}, u32[]{:S(2)}) %collective-permute-start.57) | collective-permute-done | bytes 16416 | tf_op jit(solution)/shard_map/ppermute | solution.py:33
  149.4 1.7 %collective-permute-start.58 = (f32[2,16,256]{2,1,0:T(8,128)S(1)}, f32[2,16,256]{2,1,0:T(8,128)S(1)}, u32[]{:S(2)}, u32[]{:S(2)}) collective-permute-start(f32[2,16,256]{2,1,0:T(8,128)S(1)} %pad_maximum_fusion.4), channel_id=1, source_target_pairs={{0,2},{1,3},{2,0},{3,1},{4,6},{5,7},{6,4},{7,5},{8,10},{9,11},{10,... | collective-permute-start | bytes 98312 | tf_op jit(solution)/shard_map/ppermute | solution.py:33
  151.2 3.1 %collective-permute-done.58 = f32[2,16,256]{2,1,0:T(8,128)S(1)} collective-permute-done((f32[2,16,256]{2,1,0:T(8,128)S(1)}, f32[2,16,256]{2,1,0:T(8,128)S(1)}, u32[]{:S(2)}, u32[]{:S(2)}) %collective-permute-start.58) | collective-permute-done | bytes 32800 | tf_op jit(solution)/shard_map/ppermute | solution.py:33
  (200 shorter events, 27.5 us)
Async XLA Ops:
  0.6 31.2 %copy-start = (f32[1,3,256,1024]{3,2,1,0:T(8,128)S(1)}, f32[1,3,256,1024]{3,2,1,0:T(8,128)}, u32[]{:S(2)}) copy-start(f32[1,3,256,1024]{3,2,1,0:T(8,128)} %param.12) | copy-start | bytes 9437188
  2.1 9.5 %collective-permute-start.2 = (f32[64,256]{1,0:T(8,128)S(1)}, f32[64,256]{1,0:T(8,128)S(1)}, u32[]{:S(2)}, u32[]{:S(2)}) collective-permute-start(f32[64,256]{1,0:T(8,128)S(1)} %get-tuple-element.28.refs_0_), channel_id=1, source_target_pairs={{0,3},{1,2},{2,1},{3,0},{4,7},{5,6},{6,5},{7,4},{8,11},{9,10},{10,... | collective-permute-start | bytes 196616 | tf_op jit(solution)/shard_map/ppermute | solution.py:33
  7.2 11.0 %collective-permute-start.1 = (f32[64,256]{1,0:T(8,128)S(1)}, f32[64,256]{1,0:T(8,128)}, u32[]{:S(2)}, u32[]{:S(2)}) collective-permute-start(f32[64,256]{1,0:T(8,128)S(1)} %get-tuple-element.28.refs_0_), channel_id=1, source_target_pairs={{0,2},{1,3},{2,0},{3,1},{4,6},{5,7},{6,4},{7,5},{8,10},{9,11},{10,... | collective-permute-start | bytes 196616 | tf_op jit(solution)/shard_map/ppermute | solution.py:33
  7.2 11.0 %collective-permute-start = (f32[64,256]{1,0:T(8,128)S(1)}, f32[64,256]{1,0:T(8,128)}, u32[]{:S(2)}, u32[]{:S(2)}) collective-permute-start(f32[64,256]{1,0:T(8,128)S(1)} %get-tuple-element.28.refs_0_), channel_id=1, source_target_pairs={{0,1},{1,0},{2,3},{3,2},{4,5},{5,4},{6,7},{7,6},{8,9},{9,8},{10,11... | collective-permute-start | bytes 196616 | tf_op jit(solution)/shard_map/ppermute | solution.py:33
  7.8 18.6 %collective-permute-start.5 = (f32[64,256]{1,0:T(8,128)S(1)}, f32[64,256]{1,0:T(8,128)S(1)}, u32[]{:S(2)}, u32[]{:S(2)}) collective-permute-start(f32[64,256]{1,0:T(8,128)S(1)} %get-tuple-element.29.refs_0_), channel_id=1, source_target_pairs={{0,3},{1,2},{2,1},{3,0},{4,7},{5,6},{6,5},{7,4},{8,11},{9,10},{10,... | collective-permute-start | bytes 196616 | tf_op jit(solution)/shard_map/ppermute | solution.py:33
  11.6 15.1 %collective-permute-start.4 = (f32[64,256]{1,0:T(8,128)S(1)}, f32[64,256]{1,0:T(8,128)S(1)}, u32[]{:S(2)}, u32[]{:S(2)}) collective-permute-start(f32[64,256]{1,0:T(8,128)S(1)} %get-tuple-element.29.refs_0_), channel_id=1, source_target_pairs={{0,2},{1,3},{2,0},{3,1},{4,6},{5,7},{6,4},{7,5},{8,10},{9,11},{10,... | collective-permute-start | bytes 196616 | tf_op jit(solution)/shard_map/ppermute | solution.py:33
  11.6 15.1 %collective-permute-start.3 = (f32[64,256]{1,0:T(8,128)S(1)}, f32[64,256]{1,0:T(8,128)S(1)}, u32[]{:S(2)}, u32[]{:S(2)}) collective-permute-start(f32[64,256]{1,0:T(8,128)S(1)} %get-tuple-element.29.refs_0_), channel_id=1, source_target_pairs={{0,1},{1,0},{2,3},{3,2},{4,5},{5,4},{6,7},{7,6},{8,9},{9,8},{10,11... | collective-permute-start | bytes 196616 | tf_op jit(solution)/shard_map/ppermute | solution.py:33
  22.2 9.0 %collective-permute-start.8 = (f32[64,256]{1,0:T(8,128)S(1)}, f32[64,256]{1,0:T(8,128)S(1)}, u32[]{:S(2)}, u32[]{:S(2)}) collective-permute-start(f32[64,256]{1,0:T(8,128)S(1)} %shard_map.114.refs_0_), channel_id=1, source_target_pairs={{0,1},{1,0},{2,3},{3,2},{4,5},{5,4},{6,7},{7,6},{8,9},{9,8},{10,11... | collective-permute-start | bytes 196616 | tf_op jit(solution)/shard_map/ppermute | solution.py:33
  23.5 8.6 %collective-permute-start.7 = (f32[64,256]{1,0:T(8,128)S(1)}, f32[64,256]{1,0:T(8,128)S(1)}, u32[]{:S(2)}, u32[]{:S(2)}) collective-permute-start(f32[64,256]{1,0:T(8,128)S(1)} %shard_map.114.refs_0_), channel_id=1, source_target_pairs={{0,2},{1,3},{2,0},{3,1},{4,6},{5,7},{6,4},{7,5},{8,10},{9,11},{10,... | collective-permute-start | bytes 196616 | tf_op jit(solution)/shard_map/ppermute | solution.py:33
  26.4 6.6 %collective-permute-start.6 = (f32[64,256]{1,0:T(8,128)S(1)}, f32[64,256]{1,0:T(8,128)S(1)}, u32[]{:S(2)}, u32[]{:S(2)}) collective-permute-start(f32[64,256]{1,0:T(8,128)S(1)} %shard_map.114.refs_0_), channel_id=1, source_target_pairs={{0,3},{1,2},{2,1},{3,0},{4,7},{5,6},{6,5},{7,4},{8,11},{9,10},{10,... | collective-permute-start | bytes 196616 | tf_op jit(solution)/shard_map/ppermute | solution.py:33
  27.4 9.4 %collective-permute-start.14 = (f32[64,256]{1,0:T(8,128)S(1)}, f32[64,256]{1,0:T(8,128)S(1)}, u32[]{:S(2)}, u32[]{:S(2)}) collective-permute-start(f32[64,256]{1,0:T(8,128)S(1)} %shard_map.115.refs_1_), channel_id=1, source_target_pairs={{0,1},{1,0},{2,3},{3,2},{4,5},{5,4},{6,7},{7,6},{8,9},{9,8},{10,11... | collective-permute-start | bytes 196616 | tf_op jit(solution)/shard_map/ppermute | solution.py:33
  27.8 10.8 %collective-permute-start.13 = (f32[64,256]{1,0:T(8,128)S(1)}, f32[64,256]{1,0:T(8,128)S(1)}, u32[]{:S(2)}, u32[]{:S(2)}) collective-permute-start(f32[64,256]{1,0:T(8,128)S(1)} %shard_map.115.refs_1_), channel_id=1, source_target_pairs={{0,3},{1,2},{2,1},{3,0},{4,7},{5,6},{6,5},{7,4},{8,11},{9,10},{10,... | collective-permute-start | bytes 196616 | tf_op jit(solution)/shard_map/ppermute | solution.py:33
  31.2 8.2 %collective-permute-start.12 = (f32[64,256]{1,0:T(8,128)S(1)}, f32[64,256]{1,0:T(8,128)S(1)}, u32[]{:S(2)}, u32[]{:S(2)}) collective-permute-start(f32[64,256]{1,0:T(8,128)S(1)} %shard_map.115.refs_1_), channel_id=1, source_target_pairs={{0,2},{1,3},{2,0},{3,1},{4,6},{5,7},{6,4},{7,5},{8,10},{9,11},{10,... | collective-permute-start | bytes 196616 | tf_op jit(solution)/shard_map/ppermute | solution.py:33
  33.9 11.3 %collective-permute-start.11 = (f32[64,256]{1,0:T(8,128)S(1)}, f32[64,256]{1,0:T(8,128)S(1)}, u32[]{:S(2)}, u32[]{:S(2)}) collective-permute-start(f32[64,256]{1,0:T(8,128)S(1)} %fusion.19), channel_id=1, source_target_pairs={{0,1},{1,0},{2,3},{3,2},{4,5},{5,4},{6,7},{7,6},{8,9},{9,8},{10,11... | collective-permute-start | bytes 196616 | tf_op jit(solution)/shard_map/ppermute | solution.py:33
  35.4 10.1 %collective-permute-start.10 = (f32[64,256]{1,0:T(8,128)S(1)}, f32[64,256]{1,0:T(8,128)S(1)}, u32[]{:S(2)}, u32[]{:S(2)}) collective-permute-start(f32[64,256]{1,0:T(8,128)S(1)} %fusion.19), channel_id=1, source_target_pairs={{0,2},{1,3},{2,0},{3,1},{4,6},{5,7},{6,4},{7,5},{8,10},{9,11},{10,... | collective-permute-start | bytes 196616 | tf_op jit(solution)/shard_map/ppermute | solution.py:33
  36.8 6.5 %collective-permute-start.9 = (f32[64,256]{1,0:T(8,128)S(1)}, f32[64,256]{1,0:T(8,128)S(1)}, u32[]{:S(2)}, u32[]{:S(2)}) collective-permute-start(f32[64,256]{1,0:T(8,128)S(1)} %fusion.19), channel_id=1, source_target_pairs={{0,3},{1,2},{2,1},{3,0},{4,7},{5,6},{6,5},{7,4},{8,11},{9,10},{10,... | collective-permute-start | bytes 196616 | tf_op jit(solution)/shard_map/ppermute | solution.py:33
  40.3 12.3 %collective-permute-start.17 = (f32[64,256]{1,0:T(8,128)S(1)}, f32[64,256]{1,0:T(8,128)S(1)}, u32[]{:S(2)}, u32[]{:S(2)}) collective-permute-start(f32[64,256]{1,0:T(8,128)S(1)} %fusion.15), channel_id=1, source_target_pairs={{0,1},{1,0},{2,3},{3,2},{4,5},{5,4},{6,7},{7,6},{8,9},{9,8},{10,11... | collective-permute-start | bytes 196616 | tf_op jit(solution)/shard_map/ppermute | solution.py:33
  40.4 12.5 %collective-permute-start.16 = (f32[64,256]{1,0:T(8,128)S(1)}, f32[64,256]{1,0:T(8,128)S(1)}, u32[]{:S(2)}, u32[]{:S(2)}) collective-permute-start(f32[64,256]{1,0:T(8,128)S(1)} %fusion.15), channel_id=1, source_target_pairs={{0,3},{1,2},{2,1},{3,0},{4,7},{5,6},{6,5},{7,4},{8,11},{9,10},{10,... | collective-permute-start | bytes 196616 | tf_op jit(solution)/shard_map/ppermute | solution.py:33
  43.3 7.5 %collective-permute-start.15 = (f32[64,256]{1,0:T(8,128)S(1)}, f32[64,256]{1,0:T(8,128)S(1)}, u32[]{:S(2)}, u32[]{:S(2)}) collective-permute-start(f32[64,256]{1,0:T(8,128)S(1)} %fusion.15), channel_id=1, source_target_pairs={{0,2},{1,3},{2,0},{3,1},{4,6},{5,7},{6,4},{7,5},{8,10},{9,11},{10,... | collective-permute-start | bytes 196616 | tf_op jit(solution)/shard_map/ppermute | solution.py:33
  46.1 11.9 %collective-permute-start.20 = (f32[64,256]{1,0:T(8,128)S(1)}, f32[64,256]{1,0:T(8,128)S(1)}, u32[]{:S(2)}, u32[]{:S(2)}) collective-permute-start(f32[64,256]{1,0:T(8,128)S(1)} %get-tuple-element.55.refs_2_), channel_id=1, source_target_pairs={{0,1},{1,0},{2,3},{3,2},{4,5},{5,4},{6,7},{7,6},{8,9},{9,8},{10,11... | collective-permute-start | bytes 196616 | tf_op jit(solution)/shard_map/ppermute | solution.py:33
  46.4 11.8 %collective-permute-start.19 = (f32[64,256]{1,0:T(8,128)S(1)}, f32[64,256]{1,0:T(8,128)S(1)}, u32[]{:S(2)}, u32[]{:S(2)}) collective-permute-start(f32[64,256]{1,0:T(8,128)S(1)} %get-tuple-element.55.refs_2_), channel_id=1, source_target_pairs={{0,2},{1,3},{2,0},{3,1},{4,6},{5,7},{6,4},{7,5},{8,10},{9,11},{10,... | collective-permute-start | bytes 196616 | tf_op jit(solution)/shard_map/ppermute | solution.py:33
  50.8 6.6 %collective-permute-start.18 = (f32[64,256]{1,0:T(8,128)S(1)}, f32[64,256]{1,0:T(8,128)S(1)}, u32[]{:S(2)}, u32[]{:S(2)}) collective-permute-start(f32[64,256]{1,0:T(8,128)S(1)} %get-tuple-element.55.refs_2_), channel_id=1, source_target_pairs={{0,3},{1,2},{2,1},{3,0},{4,7},{5,6},{6,5},{7,4},{8,11},{9,10},{10,... | collective-permute-start | bytes 196616 | tf_op jit(solution)/shard_map/ppermute | solution.py:33
  53.6 12.3 %collective-permute-start.26 = (f32[64,256]{1,0:T(8,128)S(1)}, f32[64,256]{1,0:T(8,128)S(1)}, u32[]{:S(2)}, u32[]{:S(2)}) collective-permute-start(f32[64,256]{1,0:T(8,128)S(1)} %get-tuple-element.61.refs_3_), channel_id=1, source_target_pairs={{0,1},{1,0},{2,3},{3,2},{4,5},{5,4},{6,7},{7,6},{8,9},{9,8},{10,11... | collective-permute-start | bytes 196616 | tf_op jit(solution)/shard_map/ppermute | solution.py:33
  53.6 12.5 %collective-permute-start.25 = (f32[64,256]{1,0:T(8,128)S(1)}, f32[64,256]{1,0:T(8,128)S(1)}, u32[]{:S(2)}, u32[]{:S(2)}) collective-permute-start(f32[64,256]{1,0:T(8,128)S(1)} %get-tuple-element.61.refs_3_), channel_id=1, source_target_pairs={{0,3},{1,2},{2,1},{3,0},{4,7},{5,6},{6,5},{7,4},{8,11},{9,10},{10,... | collective-permute-start | bytes 196616 | tf_op jit(solution)/shard_map/ppermute | solution.py:33
  57.4 6.2 %collective-permute-start.24 = (f32[64,256]{1,0:T(8,128)S(1)}, f32[64,256]{1,0:T(8,128)S(1)}, u32[]{:S(2)}, u32[]{:S(2)}) collective-permute-start(f32[64,256]{1,0:T(8,128)S(1)} %get-tuple-element.61.refs_3_), channel_id=1, source_target_pairs={{0,2},{1,3},{2,0},{3,1},{4,6},{5,7},{6,4},{7,5},{8,10},{9,11},{10,... | collective-permute-start | bytes 196616 | tf_op jit(solution)/shard_map/ppermute | solution.py:33
  58.9 11.9 %collective-permute-start.23 = (f32[64,256]{1,0:T(8,128)S(1)}, f32[64,256]{1,0:T(8,128)S(1)}, u32[]{:S(2)}, u32[]{:S(2)}) collective-permute-start(f32[64,256]{1,0:T(8,128)S(1)} %fusion.11), channel_id=1, source_target_pairs={{0,1},{1,0},{2,3},{3,2},{4,5},{5,4},{6,7},{7,6},{8,9},{9,8},{10,11... | collective-permute-start | bytes 196616 | tf_op jit(solution)/shard_map/ppermute | solution.py:33
  60.3 10.8 %collective-permute-start.22 = (f32[64,256]{1,0:T(8,128)S(1)}, f32[64,256]{1,0:T(8,128)S(1)}, u32[]{:S(2)}, u32[]{:S(2)}) collective-permute-start(f32[64,256]{1,0:T(8,128)S(1)} %fusion.11), channel_id=1, source_target_pairs={{0,2},{1,3},{2,0},{3,1},{4,6},{5,7},{6,4},{7,5},{8,10},{9,11},{10,... | collective-permute-start | bytes 196616 | tf_op jit(solution)/shard_map/ppermute | solution.py:33
  63.6 6.4 %collective-permute-start.21 = (f32[64,256]{1,0:T(8,128)S(1)}, f32[64,256]{1,0:T(8,128)S(1)}, u32[]{:S(2)}, u32[]{:S(2)}) collective-permute-start(f32[64,256]{1,0:T(8,128)S(1)} %fusion.11), channel_id=1, source_target_pairs={{0,3},{1,2},{2,1},{3,0},{4,7},{5,6},{6,5},{7,4},{8,11},{9,10},{10,... | collective-permute-start | bytes 196616 | tf_op jit(solution)/shard_map/ppermute | solution.py:33
  66.8 13.3 %collective-permute-start.29 = (f32[64,256]{1,0:T(8,128)S(1)}, f32[64,256]{1,0:T(8,128)S(1)}, u32[]{:S(2)}, u32[]{:S(2)}) collective-permute-start(f32[64,256]{1,0:T(8,128)S(1)} %fusion.8), channel_id=1, source_target_pairs={{0,1},{1,0},{2,3},{3,2},{4,5},{5,4},{6,7},{7,6},{8,9},{9,8},{10,11... | collective-permute-start | bytes 196616 | tf_op jit(solution)/shard_map/ppermute | solution.py:33
  66.8 13.5 %collective-permute-start.28 = (f32[64,256]{1,0:T(8,128)S(1)}, f32[64,256]{1,0:T(8,128)S(1)}, u32[]{:S(2)}, u32[]{:S(2)}) collective-permute-start(f32[64,256]{1,0:T(8,128)S(1)} %fusion.8), channel_id=1, source_target_pairs={{0,3},{1,2},{2,1},{3,0},{4,7},{5,6},{6,5},{7,4},{8,11},{9,10},{10,... | collective-permute-start | bytes 196616 | tf_op jit(solution)/shard_map/ppermute | solution.py:33
  70.0 7.6 %collective-permute-start.27 = (f32[64,256]{1,0:T(8,128)S(1)}, f32[64,256]{1,0:T(8,128)S(1)}, u32[]{:S(2)}, u32[]{:S(2)}) collective-permute-start(f32[64,256]{1,0:T(8,128)S(1)} %fusion.8), channel_id=1, source_target_pairs={{0,2},{1,3},{2,0},{3,1},{4,6},{5,7},{6,4},{7,5},{8,10},{9,11},{10,... | collective-permute-start | bytes 196616 | tf_op jit(solution)/shard_map/ppermute | solution.py:33
  70.8 23.0 %copy-start.13 = (f32[64,256]{1,0:T(8,128)S(1)}, f32[64,256]{1,0:T(8,128)}, u32[]{:S(2)}) copy-start(f32[64,256]{1,0:T(8,128)} %copy-done.12) | copy-start | bytes 196612
  71.7 13.1 %collective-permute-start.32 = (f32[64,256]{1,0:T(8,128)S(1)}, f32[64,256]{1,0:T(8,128)S(1)}, u32[]{:S(2)}, u32[]{:S(2)}) collective-permute-start(f32[64,256]{1,0:T(8,128)S(1)} %get-tuple-element.57.refs_4_), channel_id=1, source_target_pairs={{0,1},{1,0},{2,3},{3,2},{4,5},{5,4},{6,7},{7,6},{8,9},{9,8},{10,11... | collective-permute-start | bytes 196616 | tf_op jit(solution)/shard_map/ppermute | solution.py:33
  74.0 11.1 %collective-permute-start.31 = (f32[64,256]{1,0:T(8,128)S(1)}, f32[64,256]{1,0:T(8,128)S(1)}, u32[]{:S(2)}, u32[]{:S(2)}) collective-permute-start(f32[64,256]{1,0:T(8,128)S(1)} %get-tuple-element.57.refs_4_), channel_id=1, source_target_pairs={{0,2},{1,3},{2,0},{3,1},{4,6},{5,7},{6,4},{7,5},{8,10},{9,11},{10,... | collective-permute-start | bytes 196616 | tf_op jit(solution)/shard_map/ppermute | solution.py:33
  77.6 6.1 %collective-permute-start.30 = (f32[64,256]{1,0:T(8,128)S(1)}, f32[64,256]{1,0:T(8,128)S(1)}, u32[]{:S(2)}, u32[]{:S(2)}) collective-permute-start(f32[64,256]{1,0:T(8,128)S(1)} %get-tuple-element.57.refs_4_), channel_id=1, source_target_pairs={{0,3},{1,2},{2,1},{3,0},{4,7},{5,6},{6,5},{7,4},{8,11},{9,10},{10,... | collective-permute-start | bytes 196616 | tf_op jit(solution)/shard_map/ppermute | solution.py:33
  81.0 12.5 %collective-permute-start.38 = (f32[64,256]{1,0:T(8,128)S(1)}, f32[64,256]{1,0:T(8,128)S(1)}, u32[]{:S(2)}, u32[]{:S(2)}) collective-permute-start(f32[64,256]{1,0:T(8,128)S(1)} %get-tuple-element.63.refs_5_), channel_id=1, source_target_pairs={{0,1},{1,0},{2,3},{3,2},{4,5},{5,4},{6,7},{7,6},{8,9},{9,8},{10,11... | collective-permute-start | bytes 196616 | tf_op jit(solution)/shard_map/ppermute | solution.py:33
  81.0 12.7 %collective-permute-start.37 = (f32[64,256]{1,0:T(8,128)S(1)}, f32[64,256]{1,0:T(8,128)S(1)}, u32[]{:S(2)}, u32[]{:S(2)}) collective-permute-start(f32[64,256]{1,0:T(8,128)S(1)} %get-tuple-element.63.refs_5_), channel_id=1, source_target_pairs={{0,3},{1,2},{2,1},{3,0},{4,7},{5,6},{6,5},{7,4},{8,11},{9,10},{10,... | collective-permute-start | bytes 196616 | tf_op jit(solution)/shard_map/ppermute | solution.py:33
  83.7 7.8 %collective-permute-start.36 = (f32[64,256]{1,0:T(8,128)S(1)}, f32[64,256]{1,0:T(8,128)S(1)}, u32[]{:S(2)}, u32[]{:S(2)}) collective-permute-start(f32[64,256]{1,0:T(8,128)S(1)} %get-tuple-element.63.refs_5_), channel_id=1, source_target_pairs={{0,2},{1,3},{2,0},{3,1},{4,6},{5,7},{6,4},{7,5},{8,10},{9,11},{10,... | collective-permute-start | bytes 196616 | tf_op jit(solution)/shard_map/ppermute | solution.py:33
  85.7 24.4 %copy-start.3 = (f32[1,1,3,128,1024]{4,3,2,1,0:T(8,128)S(1)}, f32[1,1,3,128,1024]{4,3,2,1,0:T(8,128)}, u32[]{:S(2)}) copy-start(f32[1,1,3,128,1024]{4,3,2,1,0:T(8,128)} %param.13) | copy-start | bytes 4718596
  85.7 24.4 %copy-start.21 = (s32[1,1,3]{2,1,0:T(1,128)S(1)}, s32[1,1,3]{2,1,0:T(1,128)}, u32[]{:S(2)}) copy-start(s32[1,1,3]{2,1,0:T(1,128)} %refs_6_.1) | copy-start | bytes 40
  85.7 12.7 %collective-permute-start.35 = (f32[64,256]{1,0:T(8,128)S(1)}, f32[64,256]{1,0:T(8,128)S(1)}, u32[]{:S(2)}, u32[]{:S(2)}) collective-permute-start(f32[64,256]{1,0:T(8,128)S(1)} %fusion.5), channel_id=1, source_target_pairs={{0,1},{1,0},{2,3},{3,2},{4,5},{5,4},{6,7},{7,6},{8,9},{9,8},{10,11... | collective-permute-start | bytes 196616 | tf_op jit(solution)/shard_map/ppermute | solution.py:33
  87.7 11.1 %collective-permute-start.34 = (f32[64,256]{1,0:T(8,128)S(1)}, f32[64,256]{1,0:T(8,128)S(1)}, u32[]{:S(2)}, u32[]{:S(2)}) collective-permute-start(f32[64,256]{1,0:T(8,128)S(1)} %fusion.5), channel_id=1, source_target_pairs={{0,2},{1,3},{2,0},{3,1},{4,6},{5,7},{6,4},{7,5},{8,10},{9,11},{10,... | collective-permute-start | bytes 196616 | tf_op jit(solution)/shard_map/ppermute | solution.py:33
  91.5 6.6 %collective-permute-start.33 = (f32[64,256]{1,0:T(8,128)S(1)}, f32[64,256]{1,0:T(8,128)S(1)}, u32[]{:S(2)}, u32[]{:S(2)}) collective-permute-start(f32[64,256]{1,0:T(8,128)S(1)} %fusion.5), channel_id=1, source_target_pairs={{0,3},{1,2},{2,1},{3,0},{4,7},{5,6},{6,5},{7,4},{8,11},{9,10},{10,... | collective-permute-start | bytes 196616 | tf_op jit(solution)/shard_map/ppermute | solution.py:33
  94.3 11.6 %collective-permute-start.41 = (f32[64,256]{1,0:T(8,128)S(1)}, f32[64,256]{1,0:T(8,128)S(1)}, u32[]{:S(2)}, u32[]{:S(2)}) collective-permute-start(f32[64,256]{1,0:T(8,128)S(1)} %fusion.2), channel_id=1, source_target_pairs={{0,1},{1,0},{2,3},{3,2},{4,5},{5,4},{6,7},{7,6},{8,9},{9,8},{10,11... | collective-permute-start | bytes 196616 | tf_op jit(solution)/shard_map/ppermute | solution.py:33
  94.4 11.8 %collective-permute-start.40 = (f32[64,256]{1,0:T(8,128)S(1)}, f32[64,256]{1,0:T(8,128)S(1)}, u32[]{:S(2)}, u32[]{:S(2)}) collective-permute-start(f32[64,256]{1,0:T(8,128)S(1)} %fusion.2), channel_id=1, source_target_pairs={{0,3},{1,2},{2,1},{3,0},{4,7},{5,6},{6,5},{7,4},{8,11},{9,10},{10,... | collective-permute-start | bytes 196616 | tf_op jit(solution)/shard_map/ppermute | solution.py:33
  98.1 5.8 %collective-permute-start.39 = (f32[64,256]{1,0:T(8,128)S(1)}, f32[64,256]{1,0:T(8,128)S(1)}, u32[]{:S(2)}, u32[]{:S(2)}) collective-permute-start(f32[64,256]{1,0:T(8,128)S(1)} %fusion.2), channel_id=1, source_target_pairs={{0,2},{1,3},{2,0},{3,1},{4,6},{5,7},{6,4},{7,5},{8,10},{9,11},{10,... | collective-permute-start | bytes 196616 | tf_op jit(solution)/shard_map/ppermute | solution.py:33
  99.1 11.0 %collective-permute-start.44 = (f32[64,256]{1,0:T(8,128)S(1)}, f32[64,256]{1,0:T(8,128)S(1)}, u32[]{:S(2)}, u32[]{:S(2)}) collective-permute-start(f32[64,256]{1,0:T(8,128)S(1)} %get-tuple-element.59.refs_6_), channel_id=1, source_target_pairs={{0,1},{1,0},{2,3},{3,2},{4,5},{5,4},{6,7},{7,6},{8,9},{9,8},{10,11... | collective-permute-start | bytes 196616 | tf_op jit(solution)/shard_map/ppermute | solution.py:33
  101.3 8.8 %collective-permute-start.43 = (f32[64,256]{1,0:T(8,128)S(1)}, f32[64,256]{1,0:T(8,128)S(1)}, u32[]{:S(2)}, u32[]{:S(2)}) collective-permute-start(f32[64,256]{1,0:T(8,128)S(1)} %get-tuple-element.59.refs_6_), channel_id=1, source_target_pairs={{0,2},{1,3},{2,0},{3,1},{4,6},{5,7},{6,4},{7,5},{8,10},{9,11},{10,... | collective-permute-start | bytes 196616 | tf_op jit(solution)/shard_map/ppermute | solution.py:33
  104.0 6.1 %collective-permute-start.42 = (f32[64,256]{1,0:T(8,128)S(1)}, f32[64,256]{1,0:T(8,128)S(1)}, u32[]{:S(2)}, u32[]{:S(2)}) collective-permute-start(f32[64,256]{1,0:T(8,128)S(1)} %get-tuple-element.59.refs_6_), channel_id=1, source_target_pairs={{0,3},{1,2},{2,1},{3,0},{4,7},{5,6},{6,5},{7,4},{8,11},{9,10},{10,... | collective-permute-start | bytes 196616 | tf_op jit(solution)/shard_map/ppermute | solution.py:33
  106.5 8.7 %collective-permute-start.47 = (f32[64,256]{1,0:T(8,128)S(1)}, f32[64,256]{1,0:T(8,128)S(1)}, u32[]{:S(2)}, u32[]{:S(2)}) collective-permute-start(f32[64,256]{1,0:T(8,128)S(1)} %get-tuple-element.65.refs_7_), channel_id=1, source_target_pairs={{0,1},{1,0},{2,3},{3,2},{4,5},{5,4},{6,7},{7,6},{8,9},{9,8},{10,11... | collective-permute-start | bytes 196616 | tf_op jit(solution)/shard_map/ppermute | solution.py:33
  106.6 8.6 %collective-permute-start.46 = (f32[64,256]{1,0:T(8,128)S(1)}, f32[64,256]{1,0:T(8,128)S(1)}, u32[]{:S(2)}, u32[]{:S(2)}) collective-permute-start(f32[64,256]{1,0:T(8,128)S(1)} %get-tuple-element.65.refs_7_), channel_id=1, source_target_pairs={{0,3},{1,2},{2,1},{3,0},{4,7},{5,6},{6,5},{7,4},{8,11},{9,10},{10,... | collective-permute-start | bytes 196616 | tf_op jit(solution)/shard_map/ppermute | solution.py:33
  110.0 5.2 %collective-permute-start.45 = (f32[64,256]{1,0:T(8,128)S(1)}, f32[64,256]{1,0:T(8,128)S(1)}, u32[]{:S(2)}, u32[]{:S(2)}) collective-permute-start(f32[64,256]{1,0:T(8,128)S(1)} %get-tuple-element.65.refs_7_), channel_id=1, source_target_pairs={{0,2},{1,3},{2,0},{3,1},{4,6},{5,7},{6,4},{7,5},{8,10},{9,11},{10,... | collective-permute-start | bytes 196616 | tf_op jit(solution)/shard_map/ppermute | solution.py:33
  110.2 21.7 %copy-start.4 = (f32[2,256,1024]{2,1,0:T(8,128)S(1)}, f32[2,256,1024]{2,1,0:T(8,128)}, u32[]{:S(2)}) copy-start(f32[2,256,1024]{2,1,0:T(8,128)} %refs_0_.1) | copy-start | bytes 6291460
  116.8 1.4 collective-permute-start.48
  118.3 5.7 %collective-permute-start.49 = (f32[2,16,512]{2,1,0:T(8,128)S(1)}, f32[2,16,512]{2,1,0:T(8,128)S(1)}, u32[]{:S(2)}, u32[]{:S(2)}) collective-permute-start(f32[2,16,512]{2,1,0:T(8,128)S(1)} %get-tuple-element.40), channel_id=1, source_target_pairs={{0,8},{4,12},{8,0},{12,4},{16,24},{20,28},{24,16},{28,20},{1,9},{5... | collective-permute-start | bytes 196616 | tf_op jit(solution)/shard_map/ppermute | solution.py:86
  121.4 5.6 %collective-permute-start.50 = (f32[2,16,512]{2,1,0:T(8,128)S(1)}, f32[2,16,512]{2,1,0:T(8,128)S(1)}, u32[]{:S(2)}, u32[]{:S(2)}) collective-permute-start(f32[2,16,512]{2,1,0:T(8,128)S(1)} %get-tuple-element.41), channel_id=1, source_target_pairs={{0,16},{4,20},{8,24},{12,28},{16,0},{20,4},{24,8},{28,12},{1,17},{... | collective-permute-start | bytes 196616 | tf_op jit(solution)/shard_map/ppermute | solution.py:86
  121.5 5.5 %collective-permute-start.51 = (f32[2,16,512]{2,1,0:T(8,128)S(1)}, f32[2,16,512]{2,1,0:T(8,128)S(1)}, u32[]{:S(2)}, u32[]{:S(2)}) collective-permute-start(f32[2,16,512]{2,1,0:T(8,128)S(1)} %get-tuple-element.42), channel_id=1, source_target_pairs={{0,24},{4,28},{8,16},{12,20},{16,8},{20,12},{24,0},{28,4},{1,25},{... | collective-permute-start | bytes 196616 | tf_op jit(solution)/shard_map/ppermute | solution.py:86
  127.4 4.9 %collective-permute-start.52 = (f32[16,1280]{1,0:T(8,128)S(1)}, f32[16,1280]{1,0:T(8,128)S(1)}, u32[]{:S(2)}, u32[]{:S(2)}) collective-permute-start(f32[16,1280]{1,0:T(8,128)S(1)} %get-tuple-element.45), channel_id=1, source_target_pairs={{0,1},{1,0},{2,3},{3,2},{4,5},{5,4},{6,7},{7,6},{8,9},{9,8},{10,11... | collective-permute-start | bytes 245768 | tf_op jit(solution)/shard_map/ppermute | solution.py:33
  127.5 7.6 %collective-permute-start.53 = (f32[16,1280]{1,0:T(8,128)S(1)}, f32[16,1280]{1,0:T(8,128)S(1)}, u32[]{:S(2)}, u32[]{:S(2)}) collective-permute-start(f32[16,1280]{1,0:T(8,128)S(1)} %get-tuple-element.46), channel_id=1, source_target_pairs={{0,2},{1,3},{2,0},{3,1},{4,6},{5,7},{6,4},{7,5},{8,10},{9,11},{10,... | collective-permute-start | bytes 245768 | tf_op jit(solution)/shard_map/ppermute | solution.py:33
  129.7 6.3 %collective-permute-start.54 = (f32[16,1280]{1,0:T(8,128)S(1)}, f32[16,1280]{1,0:T(8,128)S(1)}, u32[]{:S(2)}, u32[]{:S(2)}) collective-permute-start(f32[16,1280]{1,0:T(8,128)S(1)} %get-tuple-element.47), channel_id=1, source_target_pairs={{0,3},{1,2},{2,1},{3,0},{4,7},{5,6},{6,5},{7,4},{8,11},{9,10},{10,... | collective-permute-start | bytes 245768 | tf_op jit(solution)/shard_map/ppermute | solution.py:33
  136.6 3.8 %collective-permute-start.55 = (f32[1,16,256]{2,1,0:T(8,128)S(1)}, f32[1,16,256]{2,1,0:T(8,128)S(1)}, u32[]{:S(2)}, u32[]{:S(2)}) collective-permute-start(f32[1,16,256]{2,1,0:T(8,128)S(1)} %bitcast.192), channel_id=1, source_target_pairs={{0,1},{1,0},{2,3},{3,2},{4,5},{5,4},{6,7},{7,6},{8,9},{9,8},{10,11... | collective-permute-start | bytes 49160 | tf_op jit(solution)/shard_map/ppermute | solution.py:33
  140.3 4.8 %collective-permute-start.56 = (f32[2,16,256]{2,1,0:T(8,128)S(1)}, f32[2,16,256]{2,1,0:T(8,128)S(1)}, u32[]{:S(2)}, u32[]{:S(2)}) collective-permute-start(f32[2,16,256]{2,1,0:T(8,128)S(1)} %pad_maximum_fusion.2), channel_id=1, source_target_pairs={{0,2},{1,3},{2,0},{3,1},{4,6},{5,7},{6,4},{7,5},{8,10},{9,11},{10,... | collective-permute-start | bytes 98312 | tf_op jit(solution)/shard_map/ppermute | solution.py:33
  145.7 3.8 %collective-permute-start.57 = (f32[1,16,256]{2,1,0:T(8,128)S(1)}, f32[1,16,256]{2,1,0:T(8,128)S(1)}, u32[]{:S(2)}, u32[]{:S(2)}) collective-permute-start(f32[1,16,256]{2,1,0:T(8,128)S(1)} %bitcast.189), channel_id=1, source_target_pairs={{0,1},{1,0},{2,3},{3,2},{4,5},{5,4},{6,7},{7,6},{8,9},{9,8},{10,11... | collective-permute-start | bytes 49160 | tf_op jit(solution)/shard_map/ppermute | solution.py:33
  149.4 4.8 %collective-permute-start.58 = (f32[2,16,256]{2,1,0:T(8,128)S(1)}, f32[2,16,256]{2,1,0:T(8,128)S(1)}, u32[]{:S(2)}, u32[]{:S(2)}) collective-permute-start(f32[2,16,256]{2,1,0:T(8,128)S(1)} %pad_maximum_fusion.4), channel_id=1, source_target_pairs={{0,2},{1,3},{2,0},{3,1},{4,6},{5,7},{6,4},{7,5},{8,10},{9,11},{10,... | collective-permute-start | bytes 98312 | tf_op jit(solution)/shard_map/ppermute | solution.py:33
  (18 other events, 151.1 us)

commit v12 on v11

--- a/solution.py
+++ b/solution.py
@@ -33,30 +33,15 @@
     return lax.ppermute(value, axis, pairs)
 
 
-def gather_rows(value, stream=0):
+def gather_rows(value):
     members = lax.axis_size("grp")
     me = lax.axis_index("grp")
     rows = value.shape[1]
     pieces = [(me * rows, value)]
-    distances = list(range(members - 1, 0, -1))
-    if stream % 2:
-        distances[:2] = distances[1::-1]
-    for distance in distances:
+    for distance in range(1, members):
         owner = partner(me, distance, members)
         pieces.append((owner * rows, send(value, "grp", distance)))
     return pieces
-
-
-def gather_small(value):
-    members = lax.axis_size("grp")
-    if members & (members - 1):
-        return [value] + [send(value, "grp", d) for d in range(1, members)]
-    held = value[None]
-    distance = 1
-    while distance < members:
-        held = jnp.concatenate([held, send(held, "grp", distance)], axis=0)
-        distance *= 2
-    return [held]
 
 
 def assemble(pieces, order):
@@ -376,16 +361,11 @@
         whole[:, j * width : (j + 1) * width] = value
 
 
-def apply_first(value, stream, factor):
+def apply_first(value, factor):
     members = lax.axis_size("grp")
     depth, width = value.shape
     rows, order = factor.shape[2:]
-    order_of = list(range(members - 1, 0, -1))
-    if stream % 2:
-        order_of[:2] = order_of[1::-1]
-    held = {0: value}
-    for distance in order_of:
-        held[distance] = send(value, "grp", distance)
+    held = [value] + [send(value, "grp", distance) for distance in range(1, members)]
 
     def body(*refs):
         factor_ref, out, whole, matrix, sem = refs[members:]
@@ -399,7 +379,7 @@
     return local_kernel(
         body,
         [float_array(depth, rows)],
-        [held[d] for d in range(members)] + [factor],
+        [*held, factor],
         [VMEM] * members + [pl.BlockSpec(memory_space=pl.ANY)],
         flops=6 * depth * rows * order,
         scratch=[
@@ -413,22 +393,17 @@
 
 def apply_split(pieces, top, rest, index, base=None, begin=0):
     members = lax.axis_size("grp")
-    part, width = pieces[0].shape[-2:]
+    part, width = pieces[0].shape
     rows, order = top.shape[1:]
     extra = [] if base is None else [base]
-    count = len(pieces)
-
-    def body(*refs):
-        top_ref, rest_ref = refs[count : count + 2]
+
+    def body(*refs):
+        top_ref, rest_ref = refs[members : members + 2]
         out, whole = refs[-2:]
-        if count == 1:
-            held = [refs[0][d] for d in range(members)]
-        else:
-            held = [refs[d][...] for d in range(members)]
-        put_in_order(held, whole)
+        put_in_order([refs[d][...] for d in range(members)], whole)
         result = split_product(whole[...], top_ref[index], rest_ref[index])
         if extra:
-            result = refs[count + 2][:, begin : begin + rows] - result
+            result = refs[members + 2][:, begin : begin + rows] - result
         out[...] = result
 
     return local_kernel(
@@ -467,12 +442,12 @@
         owned = []
         for residual in residuals:
             if current:
-                pieces = gather_rows(residual, len(owned))
+                pieces = gather_rows(residual)
                 owned.append(apply_pieces(diag_inv_local, current, pieces))
             else:
-                owned.append(apply_first(residual, len(owned), diag_inv_local))
+                owned.append(apply_first(residual, diag_inv_local))
         solved.append(owned)
-        held = [gather_rows(value, i) for i, value in enumerate(owned)]
+        held = [gather_rows(value) for value in owned]
         gathered.append([assemble(pieces, order) for pieces in held])
         if current + 1 < supernodes:
             residuals = [
@@ -495,11 +470,11 @@
     solution, left = solve_first(payloads, inverse_top, inverse_rest)
     solutions = [solution]
     for ancestor in range(1, rhs_anc.shape[0]):
-        pieces = gather_small(solutions[-1])
+        pieces = [piece for _, piece in gather_rows(solutions[-1])]
         residual = apply_split(
             pieces, below_top, below_rest, ancestor - 1, left, (ancestor - 1) * rows
         )
-        pieces = gather_small(residual)
+        pieces = [piece for _, piece in gather_rows(residual)]
         solutions.append(apply_split(pieces, inverse_top, inverse_rest, ancestor))
     solutions = jnp.swapaxes(jnp.stack(solutions), 1, 2)
     return (solution_local, solutions)

time: 156 us -> 142 us (0.910)
  waiting for transfers between devices: 42.7 us -> 16.5 us
  starting transfers between devices: 77.7 us -> 90.3 us
    ppermute x55 -> x57, waiting for transfers between devices: 38.4 us -> 11.4 us  [send(): return lax.ppermute(value, axis, pairs)]
    ppermute x55 -> x57, starting transfers between devices: 73 us -> 86.7 us  [send(): return lax.ppermute(value, axis, pairs)]
  transfers between devices with their start and end apart: 59 -> 61, of which waited for: 22 -> 12; matrix products, arithmetic and copies ran while one was open for 9% -> 10% of each run, Pallas kernels for 4% -> 4%
where the time goes in v12:
time: 142 us
  starting transfers between devices  90.3 us (64%)
  waiting for transfers between devices  16.5 us (12%)
  matrix products  13.6 us (10%)
  Pallas kernels  9.44 us (7%)
  local copies, waits for them, and re-layouts  8.63 us (6%)
  between operations  2.5 us (2%)
    ppermute x57, starting transfers between devices, send(): return lax.ppermute(value, axis, pairs)  86.7 us
    dot_general x48, matrix products, contract_last(): lax.dot_general(left, right, (((left.ndim - 1,), (right.ndim - 1,)), ((),...  13.6 us
    ppermute x57, waiting for transfers between devices, send(): return lax.ppermute(value, axis, pairs)  11.4 us
    pallas_call x13, Pallas kernels, local_kernel(): pl.pallas_call(body, out_shape=list(outs), in_specs=specs or [VMEM] * len...  9.44 us
    unnamed x46, local copies, waits for them, and re-layouts  8.19 us
    ppermute x3, waiting for transfers between devices, swap(): return lax.ppermute(value, axis, pairs)  3.69 us
    ppermute x3, starting transfers between devices, swap(): return lax.ppermute(value, axis, pairs)  3.55 us
  transfers between devices with their start and end apart: 61, of which 12 were waited for; matrix products, arithmetic and copies ran while one was open for 10% of the time, Pallas kernels for 4%

profile of v12, /device:TPU:0, one launch (start us, length us, event | category | flops | bytes accessed | tf_op | source)
XLA Modules:
  0.0 141.6 jit_solution(8137051598537426928)
XLA Ops:
  0.7 1.2 copy-done.5
  2.1 5.1 %collective-permute-start.2 = (f32[64,256]{1,0:T(8,128)S(1)}, f32[64,256]{1,0:T(8,128)S(1)}, u32[]{:S(2)}, u32[]{:S(2)}) collective-permute-start(f32[64,256]{1,0:T(8,128)S(1)} %get-tuple-element.28.refs_0_), channel_id=1, source_target_pairs={{0,3},{1,2},{2,1},{3,0},{4,7},{5,6},{6,5},{7,4},{8,11},{9,10},{10,... | collective-permute-start | bytes 196616 | tf_op jit(solution)/shard_map/ppermute | solution.py:33
  7.2 0.6 collective-permute-start
  7.8 3.7 %collective-permute-start.5 = (f32[64,256]{1,0:T(8,128)S(1)}, f32[64,256]{1,0:T(8,128)S(1)}, u32[]{:S(2)}, u32[]{:S(2)}) collective-permute-start(f32[64,256]{1,0:T(8,128)S(1)} %get-tuple-element.29.refs_0_), channel_id=1, source_target_pairs={{0,3},{1,2},{2,1},{3,0},{4,7},{5,6},{6,5},{7,4},{8,11},{9,10},{10,... | collective-permute-start | bytes 196616 | tf_op jit(solution)/shard_map/ppermute | solution.py:33
  11.6 0.8 collective-permute-start.3
  12.4 1.0 copy-done.6
  14.4 0.6 copy-done.10
  15.7 0.6 copy-done.14
  18.2 2.2 %copy-done.1 = f32[1,4,256,1024]{3,2,1,0:T(8,128)S(1)} copy-done((f32[1,4,256,1024]{3,2,1,0:T(8,128)S(1)}, f32[1,4,256,1024]{3,2,1,0:T(8,128)}, u32[]{:S(2)}) %copy-start.1) | copy-done | bytes 4194328
  20.4 1.7 %shard_map.114.refs_0_ = f32[64,256]{1,0:T(8,128)S(1)} custom-call(f32[64,256]{1,0:T(8,128)S(1)} %get-tuple-element.28.refs_0_, f32[64,256]{1,0:T(8,128)} %collective-permute-done.refs_1_, f32[64,256]{1,0:T(8,128)} %collective-permute-done.1.refs_2_, f32[64,256]{1,0:T(8,128)S(1)} %collective-permute-done.2.refs_3_, f32[1,4,256,1024]{3,2,1,0:T(8,128)S(1)} %copy-done.1), custom_call_target="tpu_custom_call" | custom-call | flops 100663296 | bytes 4521984 | tf_op jit(solution)/shard_map/pallas_call | solution.py:80
  22.2 3.6 %collective-permute-start.8 = (f32[64,256]{1,0:T(8,128)S(1)}, f32[64,256]{1,0:T(8,128)S(1)}, u32[]{:S(2)}, u32[]{:S(2)}) collective-permute-start(f32[64,256]{1,0:T(8,128)S(1)} %shard_map.114.refs_0_), channel_id=1, source_target_pairs={{0,3},{1,2},{2,1},{3,0},{4,7},{5,6},{6,5},{7,4},{8,11},{9,10},{10,... | collective-permute-start | bytes 196616 | tf_op jit(solution)/shard_map/ppermute | solution.py:33
  25.8 0.8 collective-permute-start.6
  26.7 0.7 shard_map.115.refs_1_
  27.4 3.6 %collective-permute-start.14 = (f32[64,256]{1,0:T(8,128)S(1)}, f32[64,256]{1,0:T(8,128)S(1)}, u32[]{:S(2)}, u32[]{:S(2)}) collective-permute-start(f32[64,256]{1,0:T(8,128)S(1)} %shard_map.115.refs_1_), channel_id=1, source_target_pairs={{0,3},{1,2},{2,1},{3,0},{4,7},{5,6},{6,5},{7,4},{8,11},{9,10},{10,... | collective-permute-start | bytes 196616 | tf_op jit(solution)/shard_map/ppermute | solution.py:33
  31.1 0.9 collective-permute-start.12
  33.9 3.3 %collective-permute-start.11 = (f32[64,256]{1,0:T(8,128)S(1)}, f32[64,256]{1,0:T(8,128)S(1)}, u32[]{:S(2)}, u32[]{:S(2)}) collective-permute-start(f32[64,256]{1,0:T(8,128)S(1)} %fusion.19), channel_id=1, source_target_pairs={{0,3},{1,2},{2,1},{3,0},{4,7},{5,6},{6,5},{7,4},{8,11},{9,10},{10,... | collective-permute-start | bytes 196616 | tf_op jit(solution)/shard_map/ppermute | solution.py:33
  37.2 1.2 collective-permute-start.9
  39.9 3.3 %collective-permute-start.17 = (f32[64,256]{1,0:T(8,128)S(1)}, f32[64,256]{1,0:T(8,128)S(1)}, u32[]{:S(2)}, u32[]{:S(2)}) collective-permute-start(f32[64,256]{1,0:T(8,128)S(1)} %fusion.15), channel_id=1, source_target_pairs={{0,3},{1,2},{2,1},{3,0},{4,7},{5,6},{6,5},{7,4},{8,11},{9,10},{10,... | collective-permute-start | bytes 196616 | tf_op jit(solution)/shard_map/ppermute | solution.py:33
  43.2 1.3 collective-permute-start.15
  45.7 3.3 %collective-permute-start.20 = (f32[64,256]{1,0:T(8,128)S(1)}, f32[64,256]{1,0:T(8,128)S(1)}, u32[]{:S(2)}, u32[]{:S(2)}) collective-permute-start(f32[64,256]{1,0:T(8,128)S(1)} %get-tuple-element.55.refs_2_), channel_id=1, source_target_pairs={{0,3},{1,2},{2,1},{3,0},{4,7},{5,6},{6,5},{7,4},{8,11},{9,10},{10,... | collective-permute-start | bytes 196616 | tf_op jit(solution)/shard_map/ppermute | solution.py:33
  49.0 1.6 %collective-permute-start.18 = (f32[64,256]{1,0:T(8,128)S(1)}, f32[64,256]{1,0:T(8,128)S(1)}, u32[]{:S(2)}, u32[]{:S(2)}) collective-permute-start(f32[64,256]{1,0:T(8,128)S(1)} %get-tuple-element.55.refs_2_), channel_id=1, source_target_pairs={{0,1},{1,0},{2,3},{3,2},{4,5},{5,4},{6,7},{7,6},{8,9},{9,8},{10,11... | collective-permute-start | bytes 196616 | tf_op jit(solution)/shard_map/ppermute | solution.py:33
  51.9 2.8 %collective-permute-start.26 = (f32[64,256]{1,0:T(8,128)S(1)}, f32[64,256]{1,0:T(8,128)S(1)}, u32[]{:S(2)}, u32[]{:S(2)}) collective-permute-start(f32[64,256]{1,0:T(8,128)S(1)} %get-tuple-element.61.refs_3_), channel_id=1, source_target_pairs={{0,3},{1,2},{2,1},{3,0},{4,7},{5,6},{6,5},{7,4},{8,11},{9,10},{10,... | collective-permute-start | bytes 196616 | tf_op jit(solution)/shard_map/ppermute | solution.py:33
  54.7 1.6 %collective-permute-start.24 = (f32[64,256]{1,0:T(8,128)S(1)}, f32[64,256]{1,0:T(8,128)S(1)}, u32[]{:S(2)}, u32[]{:S(2)}) collective-permute-start(f32[64,256]{1,0:T(8,128)S(1)} %get-tuple-element.61.refs_3_), channel_id=1, source_target_pairs={{0,1},{1,0},{2,3},{3,2},{4,5},{5,4},{6,7},{7,6},{8,9},{9,8},{10,11... | collective-permute-start | bytes 196616 | tf_op jit(solution)/shard_map/ppermute | solution.py:33
  57.5 2.8 %collective-permute-start.23 = (f32[64,256]{1,0:T(8,128)S(1)}, f32[64,256]{1,0:T(8,128)S(1)}, u32[]{:S(2)}, u32[]{:S(2)}) collective-permute-start(f32[64,256]{1,0:T(8,128)S(1)} %fusion.11), channel_id=1, source_target_pairs={{0,3},{1,2},{2,1},{3,0},{4,7},{5,6},{6,5},{7,4},{8,11},{9,10},{10,... | collective-permute-start | bytes 196616 | tf_op jit(solution)/shard_map/ppermute | solution.py:33
  60.3 1.6 %collective-permute-start.21 = (f32[64,256]{1,0:T(8,128)S(1)}, f32[64,256]{1,0:T(8,128)S(1)}, u32[]{:S(2)}, u32[]{:S(2)}) collective-permute-start(f32[64,256]{1,0:T(8,128)S(1)} %fusion.11), channel_id=1, source_target_pairs={{0,1},{1,0},{2,3},{3,2},{4,5},{5,4},{6,7},{7,6},{8,9},{9,8},{10,11... | collective-permute-start | bytes 196616 | tf_op jit(solution)/shard_map/ppermute | solution.py:33
  63.2 2.8 %collective-permute-start.29 = (f32[64,256]{1,0:T(8,128)S(1)}, f32[64,256]{1,0:T(8,128)S(1)}, u32[]{:S(2)}, u32[]{:S(2)}) collective-permute-start(f32[64,256]{1,0:T(8,128)S(1)} %fusion.8), channel_id=1, source_target_pairs={{0,3},{1,2},{2,1},{3,0},{4,7},{5,6},{6,5},{7,4},{8,11},{9,10},{10,... | collective-permute-start | bytes 196616 | tf_op jit(solution)/shard_map/ppermute | solution.py:33
  66.1 1.7 %collective-permute-start.27 = (f32[64,256]{1,0:T(8,128)S(1)}, f32[64,256]{1,0:T(8,128)S(1)}, u32[]{:S(2)}, u32[]{:S(2)}) collective-permute-start(f32[64,256]{1,0:T(8,128)S(1)} %fusion.8), channel_id=1, source_target_pairs={{0,1},{1,0},{2,3},{3,2},{4,5},{5,4},{6,7},{7,6},{8,9},{9,8},{10,11... | collective-permute-start | bytes 196616 | tf_op jit(solution)/shard_map/ppermute | solution.py:33
  69.0 2.8 %collective-permute-start.32 = (f32[64,256]{1,0:T(8,128)S(1)}, f32[64,256]{1,0:T(8,128)S(1)}, u32[]{:S(2)}, u32[]{:S(2)}) collective-permute-start(f32[64,256]{1,0:T(8,128)S(1)} %get-tuple-element.57.refs_4_), channel_id=1, source_target_pairs={{0,3},{1,2},{2,1},{3,0},{4,7},{5,6},{6,5},{7,4},{8,11},{9,10},{10,... | collective-permute-start | bytes 196616 | tf_op jit(solution)/shard_map/ppermute | solution.py:33
  71.9 1.6 %collective-permute-start.30 = (f32[64,256]{1,0:T(8,128)S(1)}, f32[64,256]{1,0:T(8,128)S(1)}, u32[]{:S(2)}, u32[]{:S(2)}) collective-permute-start(f32[64,256]{1,0:T(8,128)S(1)} %get-tuple-element.57.refs_4_), channel_id=1, source_target_pairs={{0,1},{1,0},{2,3},{3,2},{4,5},{5,4},{6,7},{7,6},{8,9},{9,8},{10,11... | collective-permute-start | bytes 196616 | tf_op jit(solution)/shard_map/ppermute | solution.py:33
  74.7 2.8 %collective-permute-start.38 = (f32[64,256]{1,0:T(8,128)S(1)}, f32[64,256]{1,0:T(8,128)S(1)}, u32[]{:S(2)}, u32[]{:S(2)}) collective-permute-start(f32[64,256]{1,0:T(8,128)S(1)} %get-tuple-element.63.refs_5_), channel_id=1, source_target_pairs={{0,3},{1,2},{2,1},{3,0},{4,7},{5,6},{6,5},{7,4},{8,11},{9,10},{10,... | collective-permute-start | bytes 196616 | tf_op jit(solution)/shard_map/ppermute | solution.py:33
  77.6 1.6 %collective-permute-start.36 = (f32[64,256]{1,0:T(8,128)S(1)}, f32[64,256]{1,0:T(8,128)S(1)}, u32[]{:S(2)}, u32[]{:S(2)}) collective-permute-start(f32[64,256]{1,0:T(8,128)S(1)} %get-tuple-element.63.refs_5_), channel_id=1, source_target_pairs={{0,1},{1,0},{2,3},{3,2},{4,5},{5,4},{6,7},{7,6},{8,9},{9,8},{10,11... | collective-permute-start | bytes 196616 | tf_op jit(solution)/shard_map/ppermute | solution.py:33
  80.4 2.8 %collective-permute-start.35 = (f32[64,256]{1,0:T(8,128)S(1)}, f32[64,256]{1,0:T(8,128)S(1)}, u32[]{:S(2)}, u32[]{:S(2)}) collective-permute-start(f32[64,256]{1,0:T(8,128)S(1)} %fusion.5), channel_id=1, source_target_pairs={{0,3},{1,2},{2,1},{3,0},{4,7},{5,6},{6,5},{7,4},{8,11},{9,10},{10,... | collective-permute-start | bytes 196616 | tf_op jit(solution)/shard_map/ppermute | solution.py:33
  83.2 1.6 %collective-permute-start.33 = (f32[64,256]{1,0:T(8,128)S(1)}, f32[64,256]{1,0:T(8,128)S(1)}, u32[]{:S(2)}, u32[]{:S(2)}) collective-permute-start(f32[64,256]{1,0:T(8,128)S(1)} %fusion.5), channel_id=1, source_target_pairs={{0,1},{1,0},{2,3},{3,2},{4,5},{5,4},{6,7},{7,6},{8,9},{9,8},{10,11... | collective-permute-start | bytes 196616 | tf_op jit(solution)/shard_map/ppermute | solution.py:33
  86.1 2.8 %collective-permute-start.41 = (f32[64,256]{1,0:T(8,128)S(1)}, f32[64,256]{1,0:T(8,128)S(1)}, u32[]{:S(2)}, u32[]{:S(2)}) collective-permute-start(f32[64,256]{1,0:T(8,128)S(1)} %fusion.2), channel_id=1, source_target_pairs={{0,3},{1,2},{2,1},{3,0},{4,7},{5,6},{6,5},{7,4},{8,11},{9,10},{10,... | collective-permute-start | bytes 196616 | tf_op jit(solution)/shard_map/ppermute | solution.py:33
  89.0 1.7 %collective-permute-start.39 = (f32[64,256]{1,0:T(8,128)S(1)}, f32[64,256]{1,0:T(8,128)S(1)}, u32[]{:S(2)}, u32[]{:S(2)}) collective-permute-start(f32[64,256]{1,0:T(8,128)S(1)} %fusion.2), channel_id=1, source_target_pairs={{0,1},{1,0},{2,3},{3,2},{4,5},{5,4},{6,7},{7,6},{8,9},{9,8},{10,11... | collective-permute-start | bytes 196616 | tf_op jit(solution)/shard_map/ppermute | solution.py:33
  91.6 2.8 %collective-permute-start.44 = (f32[64,256]{1,0:T(8,128)S(1)}, f32[64,256]{1,0:T(8,128)S(1)}, u32[]{:S(2)}, u32[]{:S(2)}) collective-permute-start(f32[64,256]{1,0:T(8,128)S(1)} %get-tuple-element.59.refs_6_), channel_id=1, source_target_pairs={{0,3},{1,2},{2,1},{3,0},{4,7},{5,6},{6,5},{7,4},{8,11},{9,10},{10,... | collective-permute-start | bytes 196616 | tf_op jit(solution)/shard_map/ppermute | solution.py:33
  94.5 1.6 %collective-permute-start.42 = (f32[64,256]{1,0:T(8,128)S(1)}, f32[64,256]{1,0:T(8,128)S(1)}, u32[]{:S(2)}, u32[]{:S(2)}) collective-permute-start(f32[64,256]{1,0:T(8,128)S(1)} %get-tuple-element.59.refs_6_), channel_id=1, source_target_pairs={{0,1},{1,0},{2,3},{3,2},{4,5},{5,4},{6,7},{7,6},{8,9},{9,8},{10,11... | collective-permute-start | bytes 196616 | tf_op jit(solution)/shard_map/ppermute | solution.py:33
  97.0 2.8 %collective-permute-start.47 = (f32[64,256]{1,0:T(8,128)S(1)}, f32[64,256]{1,0:T(8,128)S(1)}, u32[]{:S(2)}, u32[]{:S(2)}) collective-permute-start(f32[64,256]{1,0:T(8,128)S(1)} %get-tuple-element.65.refs_7_), channel_id=1, source_target_pairs={{0,3},{1,2},{2,1},{3,0},{4,7},{5,6},{6,5},{7,4},{8,11},{9,10},{10,... | collective-permute-start | bytes 196616 | tf_op jit(solution)/shard_map/ppermute | solution.py:33
  99.8 1.6 %collective-permute-start.45 = (f32[64,256]{1,0:T(8,128)S(1)}, f32[64,256]{1,0:T(8,128)S(1)}, u32[]{:S(2)}, u32[]{:S(2)}) collective-permute-start(f32[64,256]{1,0:T(8,128)S(1)} %get-tuple-element.65.refs_7_), channel_id=1, source_target_pairs={{0,1},{1,0},{2,3},{3,2},{4,5},{5,4},{6,7},{7,6},{8,9},{9,8},{10,11... | collective-permute-start | bytes 196616 | tf_op jit(solution)/shard_map/ppermute | solution.py:33
  101.6 1.5 %shard_map.117.refs_0_ = f32[64,384]{1,0:T(8,128)S(1)} custom-call(f32[64,1024]{1,0:T(8,128)S(1)} %constant_dynamic-update-slice_fusion.28.refs_0_, f32[64,1024]{1,0:T(8,128)S(1)} %constant_dynamic-update-slice_fusion.24.refs_1_, f32[64,1024]{1,0:T(8,128)S(1)} %constant_dynamic-update-slice_fusion.20.refs_2_, ...), custom_call_target="tpu_custom_call" | custom-call | flops 150994944 | bytes 2719756 | tf_op jit(solution)/shard_map/pallas_call | solution.py:80
  103.1 1.0 collective-permute-done.45
  104.1 0.9 collective-permute-done.46
  105.1 1.5 %shard_map.118 = (f32[4,16,512]{2,1,0:T(8,128)S(1)}, f32[4,16,512]{2,1,0:T(8,128)S(1)}) custom-call(f32[64,384]{1,0:T(8,128)S(1)} %shard_map.117.refs_0_, f32[64,1024]{1,0:T(8,128)S(1)} %constant_dynamic-update-slice_fusion.12.refs_1_, f32[64,1024]{1,0:T(8,128)S(1)} %constant_dynamic-update-slice_fusion.8.refs_2_, ...), custom_call_target="tpu_custom_call" | custom-call | flops 150994944 | bytes 2981916 | tf_op jit(solution)/shard_map/pallas_call | solution.py:80
  106.7 1.3 collective-permute-done.48.refs_1_
  108.0 1.6 %collective-permute-start.49 = (f32[2,16,512]{2,1,0:T(8,128)S(1)}, f32[2,16,512]{2,1,0:T(8,128)S(1)}, u32[]{:S(2)}, u32[]{:S(2)}) collective-permute-start(f32[2,16,512]{2,1,0:T(8,128)S(1)} %get-tuple-element.40), channel_id=1, source_target_pairs={{0,8},{4,12},{8,0},{12,4},{16,24},{20,28},{24,16},{28,20},{1,9},{5... | collective-permute-start | bytes 196616 | tf_op jit(solution)/shard_map/ppermute | solution.py:71
  109.6 1.5 %collective-permute-start.50 = (f32[2,16,512]{2,1,0:T(8,128)S(1)}, f32[2,16,512]{2,1,0:T(8,128)S(1)}, u32[]{:S(2)}, u32[]{:S(2)}) collective-permute-start(f32[2,16,512]{2,1,0:T(8,128)S(1)} %get-tuple-element.41), channel_id=1, source_target_pairs={{0,16},{4,20},{8,24},{12,28},{16,0},{20,4},{24,8},{28,12},{1,17},{... | collective-permute-start | bytes 196616 | tf_op jit(solution)/shard_map/ppermute | solution.py:71
  111.6 1.0 shard_map.119
  112.6 1.3 collective-permute-done.50.refs_2_
  113.8 2.4 %collective-permute-done.51.refs_3_ = f32[2,16,512]{2,1,0:T(8,128)S(1)} collective-permute-done((f32[2,16,512]{2,1,0:T(8,128)S(1)}, f32[2,16,512]{2,1,0:T(8,128)S(1)}, u32[]{:S(2)}, u32[]{:S(2)}) %collective-permute-start.51) | collective-permute-done | bytes 65568 | tf_op jit(solution)/shard_map/ppermute | solution.py:71
  116.7 0.8 collective-permute-start.52
  117.5 2.1 %collective-permute-start.53 = (f32[16,1280]{1,0:T(8,128)S(1)}, f32[16,1280]{1,0:T(8,128)S(1)}, u32[]{:S(2)}, u32[]{:S(2)}) collective-permute-start(f32[16,1280]{1,0:T(8,128)S(1)} %get-tuple-element.46), channel_id=1, source_target_pairs={{0,2},{1,3},{2,0},{3,1},{4,6},{5,7},{6,4},{7,5},{8,10},{9,11},{10,... | collective-permute-start | bytes 245768 | tf_op jit(solution)/shard_map/ppermute | solution.py:33
  119.6 1.5 %collective-permute-start.54 = (f32[16,1280]{1,0:T(8,128)S(1)}, f32[16,1280]{1,0:T(8,128)S(1)}, u32[]{:S(2)}, u32[]{:S(2)}) collective-permute-start(f32[16,1280]{1,0:T(8,128)S(1)} %get-tuple-element.47), channel_id=1, source_target_pairs={{0,3},{1,2},{2,1},{3,0},{4,7},{5,6},{6,5},{7,4},{8,11},{9,10},{10,... | collective-permute-start | bytes 245768 | tf_op jit(solution)/shard_map/ppermute | solution.py:33
  121.6 3.0 %collective-permute-done.53.refs_2_ = f32[16,1280]{1,0:T(8,128)S(1)} collective-permute-done((f32[16,1280]{1,0:T(8,128)S(1)}, f32[16,1280]{1,0:T(8,128)S(1)}, u32[]{:S(2)}, u32[]{:S(2)}) %collective-permute-start.53) | collective-permute-done | bytes 81952 | tf_op jit(solution)/shard_map/ppermute | solution.py:33
  124.5 1.4 collective-permute-done.54.refs_3_
  126.4 2.2 %collective-permute-start.57 = (f32[16,256]{1,0:T(8,128)S(1)}, f32[16,256]{1,0:T(8,128)S(1)}, u32[]{:S(2)}, u32[]{:S(2)}) collective-permute-start(f32[16,256]{1,0:T(8,128)S(1)} %get-tuple-element.50.refs_0_), channel_id=1, source_target_pairs={{0,3},{1,2},{2,1},{3,0},{4,7},{5,6},{6,5},{7,4},{8,11},{9,10},{10,... | collective-permute-start | bytes 49160 | tf_op jit(solution)/shard_map/ppermute | solution.py:33
  128.8 2.0 %collective-permute-start.55 = (f32[16,256]{1,0:T(8,128)S(1)}, f32[16,256]{1,0:T(8,128)S(1)}, u32[]{:S(2)}, u32[]{:S(2)}) collective-permute-start(f32[16,256]{1,0:T(8,128)S(1)} %get-tuple-element.50.refs_0_), channel_id=1, source_target_pairs={{0,1},{1,0},{2,3},{3,2},{4,5},{5,4},{6,7},{7,6},{8,9},{9,8},{10,11... | collective-permute-start | bytes 49160 | tf_op jit(solution)/shard_map/ppermute | solution.py:33
  130.8 1.1 collective-permute-done.57.refs_3_
  132.0 1.4 collective-permute-done.56.refs_2_
  133.9 1.9 %collective-permute-start.60 = (f32[16,256]{1,0:T(8,128)S(1)}, f32[16,256]{1,0:T(8,128)S(1)}, u32[]{:S(2)}, u32[]{:S(2)}) collective-permute-start(f32[16,256]{1,0:T(8,128)S(1)} %shard_map.124.refs_0_), channel_id=1, source_target_pairs={{0,3},{1,2},{2,1},{3,0},{4,7},{5,6},{6,5},{7,4},{8,11},{9,10},{10,... | collective-permute-start | bytes 49160 | tf_op jit(solution)/shard_map/ppermute | solution.py:33
  135.7 0.8 collective-permute-start.59
  136.5 1.7 %collective-permute-start.58 = (f32[16,256]{1,0:T(8,128)S(1)}, f32[16,256]{1,0:T(8,128)S(1)}, u32[]{:S(2)}, u32[]{:S(2)}) collective-permute-start(f32[16,256]{1,0:T(8,128)S(1)} %shard_map.124.refs_0_), channel_id=1, source_target_pairs={{0,1},{1,0},{2,3},{3,2},{4,5},{5,4},{6,7},{7,6},{8,9},{9,8},{10,11... | collective-permute-start | bytes 49160 | tf_op jit(solution)/shard_map/ppermute | solution.py:33
  138.3 1.1 collective-permute-done.60.refs_3_
  139.4 1.0 collective-permute-done.59.refs_2_
  140.9 0.6 maximum_bitcast_fusion
  (200 shorter events, 20.9 us)
Async XLA Ops:
  0.6 31.4 %copy-start = (f32[1,3,256,1024]{3,2,1,0:T(8,128)S(1)}, f32[1,3,256,1024]{3,2,1,0:T(8,128)}, u32[]{:S(2)}) copy-start(f32[1,3,256,1024]{3,2,1,0:T(8,128)} %param.12) | copy-start | bytes 9437188
  2.1 9.5 %collective-permute-start.2 = (f32[64,256]{1,0:T(8,128)S(1)}, f32[64,256]{1,0:T(8,128)S(1)}, u32[]{:S(2)}, u32[]{:S(2)}) collective-permute-start(f32[64,256]{1,0:T(8,128)S(1)} %get-tuple-element.28.refs_0_), channel_id=1, source_target_pairs={{0,3},{1,2},{2,1},{3,0},{4,7},{5,6},{6,5},{7,4},{8,11},{9,10},{10,... | collective-permute-start | bytes 196616 | tf_op jit(solution)/shard_map/ppermute | solution.py:33
  7.2 11.0 %collective-permute-start.1 = (f32[64,256]{1,0:T(8,128)S(1)}, f32[64,256]{1,0:T(8,128)}, u32[]{:S(2)}, u32[]{:S(2)}) collective-permute-start(f32[64,256]{1,0:T(8,128)S(1)} %get-tuple-element.28.refs_0_), channel_id=1, source_target_pairs={{0,2},{1,3},{2,0},{3,1},{4,6},{5,7},{6,4},{7,5},{8,10},{9,11},{10,... | collective-permute-start | bytes 196616 | tf_op jit(solution)/shard_map/ppermute | solution.py:33
  7.2 11.0 %collective-permute-start = (f32[64,256]{1,0:T(8,128)S(1)}, f32[64,256]{1,0:T(8,128)}, u32[]{:S(2)}, u32[]{:S(2)}) collective-permute-start(f32[64,256]{1,0:T(8,128)S(1)} %get-tuple-element.28.refs_0_), channel_id=1, source_target_pairs={{0,1},{1,0},{2,3},{3,2},{4,5},{5,4},{6,7},{7,6},{8,9},{9,8},{10,11... | collective-permute-start | bytes 196616 | tf_op jit(solution)/shard_map/ppermute | solution.py:33
  7.8 18.0 %collective-permute-start.5 = (f32[64,256]{1,0:T(8,128)S(1)}, f32[64,256]{1,0:T(8,128)S(1)}, u32[]{:S(2)}, u32[]{:S(2)}) collective-permute-start(f32[64,256]{1,0:T(8,128)S(1)} %get-tuple-element.29.refs_0_), channel_id=1, source_target_pairs={{0,3},{1,2},{2,1},{3,0},{4,7},{5,6},{6,5},{7,4},{8,11},{9,10},{10,... | collective-permute-start | bytes 196616 | tf_op jit(solution)/shard_map/ppermute | solution.py:33
  11.6 15.1 %collective-permute-start.4 = (f32[64,256]{1,0:T(8,128)S(1)}, f32[64,256]{1,0:T(8,128)S(1)}, u32[]{:S(2)}, u32[]{:S(2)}) collective-permute-start(f32[64,256]{1,0:T(8,128)S(1)} %get-tuple-element.29.refs_0_), channel_id=1, source_target_pairs={{0,2},{1,3},{2,0},{3,1},{4,6},{5,7},{6,4},{7,5},{8,10},{9,11},{10,... | collective-permute-start | bytes 196616 | tf_op jit(solution)/shard_map/ppermute | solution.py:33
  11.6 15.0 %collective-permute-start.3 = (f32[64,256]{1,0:T(8,128)S(1)}, f32[64,256]{1,0:T(8,128)S(1)}, u32[]{:S(2)}, u32[]{:S(2)}) collective-permute-start(f32[64,256]{1,0:T(8,128)S(1)} %get-tuple-element.29.refs_0_), channel_id=1, source_target_pairs={{0,1},{1,0},{2,3},{3,2},{4,5},{5,4},{6,7},{7,6},{8,9},{9,8},{10,11... | collective-permute-start | bytes 196616 | tf_op jit(solution)/shard_map/ppermute | solution.py:33
  22.2 8.9 %collective-permute-start.8 = (f32[64,256]{1,0:T(8,128)S(1)}, f32[64,256]{1,0:T(8,128)S(1)}, u32[]{:S(2)}, u32[]{:S(2)}) collective-permute-start(f32[64,256]{1,0:T(8,128)S(1)} %shard_map.114.refs_0_), channel_id=1, source_target_pairs={{0,3},{1,2},{2,1},{3,0},{4,7},{5,6},{6,5},{7,4},{8,11},{9,10},{10,... | collective-permute-start | bytes 196616 | tf_op jit(solution)/shard_map/ppermute | solution.py:33
  25.8 6.9 %collective-permute-start.7 = (f32[64,256]{1,0:T(8,128)S(1)}, f32[64,256]{1,0:T(8,128)S(1)}, u32[]{:S(2)}, u32[]{:S(2)}) collective-permute-start(f32[64,256]{1,0:T(8,128)S(1)} %shard_map.114.refs_0_), channel_id=1, source_target_pairs={{0,2},{1,3},{2,0},{3,1},{4,6},{5,7},{6,4},{7,5},{8,10},{9,11},{10,... | collective-permute-start | bytes 196616 | tf_op jit(solution)/shard_map/ppermute | solution.py:33
  25.8 7.2 %collective-permute-start.6 = (f32[64,256]{1,0:T(8,128)S(1)}, f32[64,256]{1,0:T(8,128)S(1)}, u32[]{:S(2)}, u32[]{:S(2)}) collective-permute-start(f32[64,256]{1,0:T(8,128)S(1)} %shard_map.114.refs_0_), channel_id=1, source_target_pairs={{0,1},{1,0},{2,3},{3,2},{4,5},{5,4},{6,7},{7,6},{8,9},{9,8},{10,11... | collective-permute-start | bytes 196616 | tf_op jit(solution)/shard_map/ppermute | solution.py:33
  27.4 9.8 %collective-permute-start.14 = (f32[64,256]{1,0:T(8,128)S(1)}, f32[64,256]{1,0:T(8,128)S(1)}, u32[]{:S(2)}, u32[]{:S(2)}) collective-permute-start(f32[64,256]{1,0:T(8,128)S(1)} %shard_map.115.refs_1_), channel_id=1, source_target_pairs={{0,3},{1,2},{2,1},{3,0},{4,7},{5,6},{6,5},{7,4},{8,11},{9,10},{10,... | collective-permute-start | bytes 196616 | tf_op jit(solution)/shard_map/ppermute | solution.py:33
  31.0 7.6 %collective-permute-start.13 = (f32[64,256]{1,0:T(8,128)S(1)}, f32[64,256]{1,0:T(8,128)S(1)}, u32[]{:S(2)}, u32[]{:S(2)}) collective-permute-start(f32[64,256]{1,0:T(8,128)S(1)} %shard_map.115.refs_1_), channel_id=1, source_target_pairs={{0,2},{1,3},{2,0},{3,1},{4,6},{5,7},{6,4},{7,5},{8,10},{9,11},{10,... | collective-permute-start | bytes 196616 | tf_op jit(solution)/shard_map/ppermute | solution.py:33
  31.1 7.8 %collective-permute-start.12 = (f32[64,256]{1,0:T(8,128)S(1)}, f32[64,256]{1,0:T(8,128)S(1)}, u32[]{:S(2)}, u32[]{:S(2)}) collective-permute-start(f32[64,256]{1,0:T(8,128)S(1)} %shard_map.115.refs_1_), channel_id=1, source_target_pairs={{0,1},{1,0},{2,3},{3,2},{4,5},{5,4},{6,7},{7,6},{8,9},{9,8},{10,11... | collective-permute-start | bytes 196616 | tf_op jit(solution)/shard_map/ppermute | solution.py:33
  33.9 10.9 %collective-permute-start.11 = (f32[64,256]{1,0:T(8,128)S(1)}, f32[64,256]{1,0:T(8,128)S(1)}, u32[]{:S(2)}, u32[]{:S(2)}) collective-permute-start(f32[64,256]{1,0:T(8,128)S(1)} %fusion.19), channel_id=1, source_target_pairs={{0,3},{1,2},{2,1},{3,0},{4,7},{5,6},{6,5},{7,4},{8,11},{9,10},{10,... | collective-permute-start | bytes 196616 | tf_op jit(solution)/shard_map/ppermute | solution.py:33
  37.2 7.9 %collective-permute-start.10 = (f32[64,256]{1,0:T(8,128)S(1)}, f32[64,256]{1,0:T(8,128)S(1)}, u32[]{:S(2)}, u32[]{:S(2)}) collective-permute-start(f32[64,256]{1,0:T(8,128)S(1)} %fusion.19), channel_id=1, source_target_pairs={{0,2},{1,3},{2,0},{3,1},{4,6},{5,7},{6,4},{7,5},{8,10},{9,11},{10,... | collective-permute-start | bytes 196616 | tf_op jit(solution)/shard_map/ppermute | solution.py:33
  37.2 6.1 %collective-permute-start.9 = (f32[64,256]{1,0:T(8,128)S(1)}, f32[64,256]{1,0:T(8,128)S(1)}, u32[]{:S(2)}, u32[]{:S(2)}) collective-permute-start(f32[64,256]{1,0:T(8,128)S(1)} %fusion.19), channel_id=1, source_target_pairs={{0,1},{1,0},{2,3},{3,2},{4,5},{5,4},{6,7},{7,6},{8,9},{9,8},{10,11... | collective-permute-start | bytes 196616 | tf_op jit(solution)/shard_map/ppermute | solution.py:33
  39.9 11.1 %collective-permute-start.17 = (f32[64,256]{1,0:T(8,128)S(1)}, f32[64,256]{1,0:T(8,128)S(1)}, u32[]{:S(2)}, u32[]{:S(2)}) collective-permute-start(f32[64,256]{1,0:T(8,128)S(1)} %fusion.15), channel_id=1, source_target_pairs={{0,3},{1,2},{2,1},{3,0},{4,7},{5,6},{6,5},{7,4},{8,11},{9,10},{10,... | collective-permute-start | bytes 196616 | tf_op jit(solution)/shard_map/ppermute | solution.py:33
  43.1 8.1 %collective-permute-start.16 = (f32[64,256]{1,0:T(8,128)S(1)}, f32[64,256]{1,0:T(8,128)S(1)}, u32[]{:S(2)}, u32[]{:S(2)}) collective-permute-start(f32[64,256]{1,0:T(8,128)S(1)} %fusion.15), channel_id=1, source_target_pairs={{0,2},{1,3},{2,0},{3,1},{4,6},{5,7},{6,4},{7,5},{8,10},{9,11},{10,... | collective-permute-start | bytes 196616 | tf_op jit(solution)/shard_map/ppermute | solution.py:33
  43.2 5.8 %collective-permute-start.15 = (f32[64,256]{1,0:T(8,128)S(1)}, f32[64,256]{1,0:T(8,128)S(1)}, u32[]{:S(2)}, u32[]{:S(2)}) collective-permute-start(f32[64,256]{1,0:T(8,128)S(1)} %fusion.15), channel_id=1, source_target_pairs={{0,1},{1,0},{2,3},{3,2},{4,5},{5,4},{6,7},{7,6},{8,9},{9,8},{10,11... | collective-permute-start | bytes 196616 | tf_op jit(solution)/shard_map/ppermute | solution.py:33
  45.7 10.9 %collective-permute-start.20 = (f32[64,256]{1,0:T(8,128)S(1)}, f32[64,256]{1,0:T(8,128)S(1)}, u32[]{:S(2)}, u32[]{:S(2)}) collective-permute-start(f32[64,256]{1,0:T(8,128)S(1)} %get-tuple-element.55.refs_2_), channel_id=1, source_target_pairs={{0,3},{1,2},{2,1},{3,0},{4,7},{5,6},{6,5},{7,4},{8,11},{9,10},{10,... | collective-permute-start | bytes 196616 | tf_op jit(solution)/shard_map/ppermute | solution.py:33
  49.0 7.9 %collective-permute-start.19 = (f32[64,256]{1,0:T(8,128)S(1)}, f32[64,256]{1,0:T(8,128)S(1)}, u32[]{:S(2)}, u32[]{:S(2)}) collective-permute-start(f32[64,256]{1,0:T(8,128)S(1)} %get-tuple-element.55.refs_2_), channel_id=1, source_target_pairs={{0,2},{1,3},{2,0},{3,1},{4,6},{5,7},{6,4},{7,5},{8,10},{9,11},{10,... | collective-permute-start | bytes 196616 | tf_op jit(solution)/shard_map/ppermute | solution.py:33
  49.0 5.7 %collective-permute-start.18 = (f32[64,256]{1,0:T(8,128)S(1)}, f32[64,256]{1,0:T(8,128)S(1)}, u32[]{:S(2)}, u32[]{:S(2)}) collective-permute-start(f32[64,256]{1,0:T(8,128)S(1)} %get-tuple-element.55.refs_2_), channel_id=1, source_target_pairs={{0,1},{1,0},{2,3},{3,2},{4,5},{5,4},{6,7},{7,6},{8,9},{9,8},{10,11... | collective-permute-start | bytes 196616 | tf_op jit(solution)/shard_map/ppermute | solution.py:33
  51.9 10.4 %collective-permute-start.26 = (f32[64,256]{1,0:T(8,128)S(1)}, f32[64,256]{1,0:T(8,128)S(1)}, u32[]{:S(2)}, u32[]{:S(2)}) collective-permute-start(f32[64,256]{1,0:T(8,128)S(1)} %get-tuple-element.61.refs_3_), channel_id=1, source_target_pairs={{0,3},{1,2},{2,1},{3,0},{4,7},{5,6},{6,5},{7,4},{8,11},{9,10},{10,... | collective-permute-start | bytes 196616 | tf_op jit(solution)/shard_map/ppermute | solution.py:33
  54.7 7.9 %collective-permute-start.25 = (f32[64,256]{1,0:T(8,128)S(1)}, f32[64,256]{1,0:T(8,128)S(1)}, u32[]{:S(2)}, u32[]{:S(2)}) collective-permute-start(f32[64,256]{1,0:T(8,128)S(1)} %get-tuple-element.61.refs_3_), channel_id=1, source_target_pairs={{0,2},{1,3},{2,0},{3,1},{4,6},{5,7},{6,4},{7,5},{8,10},{9,11},{10,... | collective-permute-start | bytes 196616 | tf_op jit(solution)/shard_map/ppermute | solution.py:33
  54.7 5.7 %collective-permute-start.24 = (f32[64,256]{1,0:T(8,128)S(1)}, f32[64,256]{1,0:T(8,128)S(1)}, u32[]{:S(2)}, u32[]{:S(2)}) collective-permute-start(f32[64,256]{1,0:T(8,128)S(1)} %get-tuple-element.61.refs_3_), channel_id=1, source_target_pairs={{0,1},{1,0},{2,3},{3,2},{4,5},{5,4},{6,7},{7,6},{8,9},{9,8},{10,11... | collective-permute-start | bytes 196616 | tf_op jit(solution)/shard_map/ppermute | solution.py:33
  57.5 10.6 %collective-permute-start.23 = (f32[64,256]{1,0:T(8,128)S(1)}, f32[64,256]{1,0:T(8,128)S(1)}, u32[]{:S(2)}, u32[]{:S(2)}) collective-permute-start(f32[64,256]{1,0:T(8,128)S(1)} %fusion.11), channel_id=1, source_target_pairs={{0,3},{1,2},{2,1},{3,0},{4,7},{5,6},{6,5},{7,4},{8,11},{9,10},{10,... | collective-permute-start | bytes 196616 | tf_op jit(solution)/shard_map/ppermute | solution.py:33
  60.3 8.1 %collective-permute-start.22 = (f32[64,256]{1,0:T(8,128)S(1)}, f32[64,256]{1,0:T(8,128)S(1)}, u32[]{:S(2)}, u32[]{:S(2)}) collective-permute-start(f32[64,256]{1,0:T(8,128)S(1)} %fusion.11), channel_id=1, source_target_pairs={{0,2},{1,3},{2,0},{3,1},{4,6},{5,7},{6,4},{7,5},{8,10},{9,11},{10,... | collective-permute-start | bytes 196616 | tf_op jit(solution)/shard_map/ppermute | solution.py:33
  60.3 5.8 %collective-permute-start.21 = (f32[64,256]{1,0:T(8,128)S(1)}, f32[64,256]{1,0:T(8,128)S(1)}, u32[]{:S(2)}, u32[]{:S(2)}) collective-permute-start(f32[64,256]{1,0:T(8,128)S(1)} %fusion.11), channel_id=1, source_target_pairs={{0,1},{1,0},{2,3},{3,2},{4,5},{5,4},{6,7},{7,6},{8,9},{9,8},{10,11... | collective-permute-start | bytes 196616 | tf_op jit(solution)/shard_map/ppermute | solution.py:33
  63.2 10.6 %collective-permute-start.29 = (f32[64,256]{1,0:T(8,128)S(1)}, f32[64,256]{1,0:T(8,128)S(1)}, u32[]{:S(2)}, u32[]{:S(2)}) collective-permute-start(f32[64,256]{1,0:T(8,128)S(1)} %fusion.8), channel_id=1, source_target_pairs={{0,3},{1,2},{2,1},{3,0},{4,7},{5,6},{6,5},{7,4},{8,11},{9,10},{10,... | collective-permute-start | bytes 196616 | tf_op jit(solution)/shard_map/ppermute | solution.py:33
  66.0 8.1 %collective-permute-start.28 = (f32[64,256]{1,0:T(8,128)S(1)}, f32[64,256]{1,0:T(8,128)S(1)}, u32[]{:S(2)}, u32[]{:S(2)}) collective-permute-start(f32[64,256]{1,0:T(8,128)S(1)} %fusion.8), channel_id=1, source_target_pairs={{0,2},{1,3},{2,0},{3,1},{4,6},{5,7},{6,4},{7,5},{8,10},{9,11},{10,... | collective-permute-start | bytes 196616 | tf_op jit(solution)/shard_map/ppermute | solution.py:33
  66.1 5.7 %collective-permute-start.27 = (f32[64,256]{1,0:T(8,128)S(1)}, f32[64,256]{1,0:T(8,128)S(1)}, u32[]{:S(2)}, u32[]{:S(2)}) collective-permute-start(f32[64,256]{1,0:T(8,128)S(1)} %fusion.8), channel_id=1, source_target_pairs={{0,1},{1,0},{2,3},{3,2},{4,5},{5,4},{6,7},{7,6},{8,9},{9,8},{10,11... | collective-permute-start | bytes 196616 | tf_op jit(solution)/shard_map/ppermute | solution.py:33
  69.0 10.4 %collective-permute-start.32 = (f32[64,256]{1,0:T(8,128)S(1)}, f32[64,256]{1,0:T(8,128)S(1)}, u32[]{:S(2)}, u32[]{:S(2)}) collective-permute-start(f32[64,256]{1,0:T(8,128)S(1)} %get-tuple-element.57.refs_4_), channel_id=1, source_target_pairs={{0,3},{1,2},{2,1},{3,0},{4,7},{5,6},{6,5},{7,4},{8,11},{9,10},{10,... | collective-permute-start | bytes 196616 | tf_op jit(solution)/shard_map/ppermute | solution.py:33
  71.9 7.9 %collective-permute-start.31 = (f32[64,256]{1,0:T(8,128)S(1)}, f32[64,256]{1,0:T(8,128)S(1)}, u32[]{:S(2)}, u32[]{:S(2)}) collective-permute-start(f32[64,256]{1,0:T(8,128)S(1)} %get-tuple-element.57.refs_4_), channel_id=1, source_target_pairs={{0,2},{1,3},{2,0},{3,1},{4,6},{5,7},{6,4},{7,5},{8,10},{9,11},{10,... | collective-permute-start | bytes 196616 | tf_op jit(solution)/shard_map/ppermute | solution.py:33
  71.9 5.7 %collective-permute-start.30 = (f32[64,256]{1,0:T(8,128)S(1)}, f32[64,256]{1,0:T(8,128)S(1)}, u32[]{:S(2)}, u32[]{:S(2)}) collective-permute-start(f32[64,256]{1,0:T(8,128)S(1)} %get-tuple-element.57.refs_4_), channel_id=1, source_target_pairs={{0,1},{1,0},{2,3},{3,2},{4,5},{5,4},{6,7},{7,6},{8,9},{9,8},{10,11... | collective-permute-start | bytes 196616 | tf_op jit(solution)/shard_map/ppermute | solution.py:33
  74.7 10.4 %collective-permute-start.38 = (f32[64,256]{1,0:T(8,128)S(1)}, f32[64,256]{1,0:T(8,128)S(1)}, u32[]{:S(2)}, u32[]{:S(2)}) collective-permute-start(f32[64,256]{1,0:T(8,128)S(1)} %get-tuple-element.63.refs_5_), channel_id=1, source_target_pairs={{0,3},{1,2},{2,1},{3,0},{4,7},{5,6},{6,5},{7,4},{8,11},{9,10},{10,... | collective-permute-start | bytes 196616 | tf_op jit(solution)/shard_map/ppermute | solution.py:33
  77.5 7.9 %collective-permute-start.37 = (f32[64,256]{1,0:T(8,128)S(1)}, f32[64,256]{1,0:T(8,128)S(1)}, u32[]{:S(2)}, u32[]{:S(2)}) collective-permute-start(f32[64,256]{1,0:T(8,128)S(1)} %get-tuple-element.63.refs_5_), channel_id=1, source_target_pairs={{0,2},{1,3},{2,0},{3,1},{4,6},{5,7},{6,4},{7,5},{8,10},{9,11},{10,... | collective-permute-start | bytes 196616 | tf_op jit(solution)/shard_map/ppermute | solution.py:33
  77.6 5.7 %collective-permute-start.36 = (f32[64,256]{1,0:T(8,128)S(1)}, f32[64,256]{1,0:T(8,128)S(1)}, u32[]{:S(2)}, u32[]{:S(2)}) collective-permute-start(f32[64,256]{1,0:T(8,128)S(1)} %get-tuple-element.63.refs_5_), channel_id=1, source_target_pairs={{0,1},{1,0},{2,3},{3,2},{4,5},{5,4},{6,7},{7,6},{8,9},{9,8},{10,11... | collective-permute-start | bytes 196616 | tf_op jit(solution)/shard_map/ppermute | solution.py:33
  80.4 21.2 %copy-start.3 = (f32[1,1,3,128,1024]{4,3,2,1,0:T(8,128)S(1)}, f32[1,1,3,128,1024]{4,3,2,1,0:T(8,128)}, u32[]{:S(2)}) copy-start(f32[1,1,3,128,1024]{4,3,2,1,0:T(8,128)} %param.13) | copy-start | bytes 4718596
  80.4 21.2 %copy-start.21 = (s32[1,1,3]{2,1,0:T(1,128)S(1)}, s32[1,1,3]{2,1,0:T(1,128)}, u32[]{:S(2)}) copy-start(s32[1,1,3]{2,1,0:T(1,128)} %refs_6_.1) | copy-start | bytes 40
  80.4 10.6 %collective-permute-start.35 = (f32[64,256]{1,0:T(8,128)S(1)}, f32[64,256]{1,0:T(8,128)S(1)}, u32[]{:S(2)}, u32[]{:S(2)}) collective-permute-start(f32[64,256]{1,0:T(8,128)S(1)} %fusion.5), channel_id=1, source_target_pairs={{0,3},{1,2},{2,1},{3,0},{4,7},{5,6},{6,5},{7,4},{8,11},{9,10},{10,... | collective-permute-start | bytes 196616 | tf_op jit(solution)/shard_map/ppermute | solution.py:33
  83.2 8.1 %collective-permute-start.34 = (f32[64,256]{1,0:T(8,128)S(1)}, f32[64,256]{1,0:T(8,128)S(1)}, u32[]{:S(2)}, u32[]{:S(2)}) collective-permute-start(f32[64,256]{1,0:T(8,128)S(1)} %fusion.5), channel_id=1, source_target_pairs={{0,2},{1,3},{2,0},{3,1},{4,6},{5,7},{6,4},{7,5},{8,10},{9,11},{10,... | collective-permute-start | bytes 196616 | tf_op jit(solution)/shard_map/ppermute | solution.py:33
  83.2 5.8 %collective-permute-start.33 = (f32[64,256]{1,0:T(8,128)S(1)}, f32[64,256]{1,0:T(8,128)S(1)}, u32[]{:S(2)}, u32[]{:S(2)}) collective-permute-start(f32[64,256]{1,0:T(8,128)S(1)} %fusion.5), channel_id=1, source_target_pairs={{0,1},{1,0},{2,3},{3,2},{4,5},{5,4},{6,7},{7,6},{8,9},{9,8},{10,11... | collective-permute-start | bytes 196616 | tf_op jit(solution)/shard_map/ppermute | solution.py:33
  86.1 10.3 %collective-permute-start.41 = (f32[64,256]{1,0:T(8,128)S(1)}, f32[64,256]{1,0:T(8,128)S(1)}, u32[]{:S(2)}, u32[]{:S(2)}) collective-permute-start(f32[64,256]{1,0:T(8,128)S(1)} %fusion.2), channel_id=1, source_target_pairs={{0,3},{1,2},{2,1},{3,0},{4,7},{5,6},{6,5},{7,4},{8,11},{9,10},{10,... | collective-permute-start | bytes 196616 | tf_op jit(solution)/shard_map/ppermute | solution.py:33
  88.9 7.8 %collective-permute-start.40 = (f32[64,256]{1,0:T(8,128)S(1)}, f32[64,256]{1,0:T(8,128)S(1)}, u32[]{:S(2)}, u32[]{:S(2)}) collective-permute-start(f32[64,256]{1,0:T(8,128)S(1)} %fusion.2), channel_id=1, source_target_pairs={{0,2},{1,3},{2,0},{3,1},{4,6},{5,7},{6,4},{7,5},{8,10},{9,11},{10,... | collective-permute-start | bytes 196616 | tf_op jit(solution)/shard_map/ppermute | solution.py:33
  89.0 5.5 %collective-permute-start.39 = (f32[64,256]{1,0:T(8,128)S(1)}, f32[64,256]{1,0:T(8,128)S(1)}, u32[]{:S(2)}, u32[]{:S(2)}) collective-permute-start(f32[64,256]{1,0:T(8,128)S(1)} %fusion.2), channel_id=1, source_target_pairs={{0,1},{1,0},{2,3},{3,2},{4,5},{5,4},{6,7},{7,6},{8,9},{9,8},{10,11... | collective-permute-start | bytes 196616 | tf_op jit(solution)/shard_map/ppermute | solution.py:33
  91.6 9.9 %collective-permute-start.44 = (f32[64,256]{1,0:T(8,128)S(1)}, f32[64,256]{1,0:T(8,128)S(1)}, u32[]{:S(2)}, u32[]{:S(2)}) collective-permute-start(f32[64,256]{1,0:T(8,128)S(1)} %get-tuple-element.59.refs_6_), channel_id=1, source_target_pairs={{0,3},{1,2},{2,1},{3,0},{4,7},{5,6},{6,5},{7,4},{8,11},{9,10},{10,... | collective-permute-start | bytes 196616 | tf_op jit(solution)/shard_map/ppermute | solution.py:33
  94.5 7.0 %collective-permute-start.43 = (f32[64,256]{1,0:T(8,128)S(1)}, f32[64,256]{1,0:T(8,128)S(1)}, u32[]{:S(2)}, u32[]{:S(2)}) collective-permute-start(f32[64,256]{1,0:T(8,128)S(1)} %get-tuple-element.59.refs_6_), channel_id=1, source_target_pairs={{0,2},{1,3},{2,0},{3,1},{4,6},{5,7},{6,4},{7,5},{8,10},{9,11},{10,... | collective-permute-start | bytes 196616 | tf_op jit(solution)/shard_map/ppermute | solution.py:33
  94.5 5.4 %collective-permute-start.42 = (f32[64,256]{1,0:T(8,128)S(1)}, f32[64,256]{1,0:T(8,128)S(1)}, u32[]{:S(2)}, u32[]{:S(2)}) collective-permute-start(f32[64,256]{1,0:T(8,128)S(1)} %get-tuple-element.59.refs_6_), channel_id=1, source_target_pairs={{0,1},{1,0},{2,3},{3,2},{4,5},{5,4},{6,7},{7,6},{8,9},{9,8},{10,11... | collective-permute-start | bytes 196616 | tf_op jit(solution)/shard_map/ppermute | solution.py:33
  97.0 8.0 %collective-permute-start.47 = (f32[64,256]{1,0:T(8,128)S(1)}, f32[64,256]{1,0:T(8,128)S(1)}, u32[]{:S(2)}, u32[]{:S(2)}) collective-permute-start(f32[64,256]{1,0:T(8,128)S(1)} %get-tuple-element.65.refs_7_), channel_id=1, source_target_pairs={{0,3},{1,2},{2,1},{3,0},{4,7},{5,6},{6,5},{7,4},{8,11},{9,10},{10,... | collective-permute-start | bytes 196616 | tf_op jit(solution)/shard_map/ppermute | solution.py:33
  99.8 5.2 %collective-permute-start.46 = (f32[64,256]{1,0:T(8,128)S(1)}, f32[64,256]{1,0:T(8,128)S(1)}, u32[]{:S(2)}, u32[]{:S(2)}) collective-permute-start(f32[64,256]{1,0:T(8,128)S(1)} %get-tuple-element.65.refs_7_), channel_id=1, source_target_pairs={{0,2},{1,3},{2,0},{3,1},{4,6},{5,7},{6,4},{7,5},{8,10},{9,11},{10,... | collective-permute-start | bytes 196616 | tf_op jit(solution)/shard_map/ppermute | solution.py:33
  99.8 4.3 %collective-permute-start.45 = (f32[64,256]{1,0:T(8,128)S(1)}, f32[64,256]{1,0:T(8,128)S(1)}, u32[]{:S(2)}, u32[]{:S(2)}) collective-permute-start(f32[64,256]{1,0:T(8,128)S(1)} %get-tuple-element.65.refs_7_), channel_id=1, source_target_pairs={{0,1},{1,0},{2,3},{3,2},{4,5},{5,4},{6,7},{7,6},{8,9},{9,8},{10,11... | collective-permute-start | bytes 196616 | tf_op jit(solution)/shard_map/ppermute | solution.py:33
  106.6 1.4 collective-permute-start.48
  108.0 4.6 %collective-permute-start.49 = (f32[2,16,512]{2,1,0:T(8,128)S(1)}, f32[2,16,512]{2,1,0:T(8,128)S(1)}, u32[]{:S(2)}, u32[]{:S(2)}) collective-permute-start(f32[2,16,512]{2,1,0:T(8,128)S(1)} %get-tuple-element.40), channel_id=1, source_target_pairs={{0,8},{4,12},{8,0},{12,4},{16,24},{20,28},{24,16},{28,20},{1,9},{5... | collective-permute-start | bytes 196616 | tf_op jit(solution)/shard_map/ppermute | solution.py:71
  109.6 4.3 %collective-permute-start.50 = (f32[2,16,512]{2,1,0:T(8,128)S(1)}, f32[2,16,512]{2,1,0:T(8,128)S(1)}, u32[]{:S(2)}, u32[]{:S(2)}) collective-permute-start(f32[2,16,512]{2,1,0:T(8,128)S(1)} %get-tuple-element.41), channel_id=1, source_target_pairs={{0,16},{4,20},{8,24},{12,28},{16,0},{20,4},{24,8},{28,12},{1,17},{... | collective-permute-start | bytes 196616 | tf_op jit(solution)/shard_map/ppermute | solution.py:71
  111.1 5.2 %collective-permute-start.51 = (f32[2,16,512]{2,1,0:T(8,128)S(1)}, f32[2,16,512]{2,1,0:T(8,128)S(1)}, u32[]{:S(2)}, u32[]{:S(2)}) collective-permute-start(f32[2,16,512]{2,1,0:T(8,128)S(1)} %get-tuple-element.42), channel_id=1, source_target_pairs={{0,24},{4,28},{8,16},{12,20},{16,8},{20,12},{24,0},{28,4},{1,25},{... | collective-permute-start | bytes 196616 | tf_op jit(solution)/shard_map/ppermute | solution.py:71
  116.7 4.9 %collective-permute-start.52 = (f32[16,1280]{1,0:T(8,128)S(1)}, f32[16,1280]{1,0:T(8,128)S(1)}, u32[]{:S(2)}, u32[]{:S(2)}) collective-permute-start(f32[16,1280]{1,0:T(8,128)S(1)} %get-tuple-element.45), channel_id=1, source_target_pairs={{0,1},{1,0},{2,3},{3,2},{4,5},{5,4},{6,7},{7,6},{8,9},{9,8},{10,11... | collective-permute-start | bytes 245768 | tf_op jit(solution)/shard_map/ppermute | solution.py:33
  117.5 7.1 %collective-permute-start.53 = (f32[16,1280]{1,0:T(8,128)S(1)}, f32[16,1280]{1,0:T(8,128)S(1)}, u32[]{:S(2)}, u32[]{:S(2)}) collective-permute-start(f32[16,1280]{1,0:T(8,128)S(1)} %get-tuple-element.46), channel_id=1, source_target_pairs={{0,2},{1,3},{2,0},{3,1},{4,6},{5,7},{6,4},{7,5},{8,10},{9,11},{10,... | collective-permute-start | bytes 245768 | tf_op jit(solution)/shard_map/ppermute | solution.py:33
  119.6 6.3 %collective-permute-start.54 = (f32[16,1280]{1,0:T(8,128)S(1)}, f32[16,1280]{1,0:T(8,128)S(1)}, u32[]{:S(2)}, u32[]{:S(2)}) collective-permute-start(f32[16,1280]{1,0:T(8,128)S(1)} %get-tuple-element.47), channel_id=1, source_target_pairs={{0,3},{1,2},{2,1},{3,0},{4,7},{5,6},{6,5},{7,4},{8,11},{9,10},{10,... | collective-permute-start | bytes 245768 | tf_op jit(solution)/shard_map/ppermute | solution.py:33
  126.4 5.6 %collective-permute-start.57 = (f32[16,256]{1,0:T(8,128)S(1)}, f32[16,256]{1,0:T(8,128)S(1)}, u32[]{:S(2)}, u32[]{:S(2)}) collective-permute-start(f32[16,256]{1,0:T(8,128)S(1)} %get-tuple-element.50.refs_0_), channel_id=1, source_target_pairs={{0,3},{1,2},{2,1},{3,0},{4,7},{5,6},{6,5},{7,4},{8,11},{9,10},{10,... | collective-permute-start | bytes 49160 | tf_op jit(solution)/shard_map/ppermute | solution.py:33
  128.6 4.8 %collective-permute-start.56 = (f32[16,256]{1,0:T(8,128)S(1)}, f32[16,256]{1,0:T(8,128)S(1)}, u32[]{:S(2)}, u32[]{:S(2)}) collective-permute-start(f32[16,256]{1,0:T(8,128)S(1)} %get-tuple-element.50.refs_0_), channel_id=1, source_target_pairs={{0,2},{1,3},{2,0},{3,1},{4,6},{5,7},{6,4},{7,5},{8,10},{9,11},{10,... | collective-permute-start | bytes 49160 | tf_op jit(solution)/shard_map/ppermute | solution.py:33
  128.8 4.5 %collective-permute-start.55 = (f32[16,256]{1,0:T(8,128)S(1)}, f32[16,256]{1,0:T(8,128)S(1)}, u32[]{:S(2)}, u32[]{:S(2)}) collective-permute-start(f32[16,256]{1,0:T(8,128)S(1)} %get-tuple-element.50.refs_0_), channel_id=1, source_target_pairs={{0,1},{1,0},{2,3},{3,2},{4,5},{5,4},{6,7},{7,6},{8,9},{9,8},{10,11... | collective-permute-start | bytes 49160 | tf_op jit(solution)/shard_map/ppermute | solution.py:33
  133.9 5.6 %collective-permute-start.60 = (f32[16,256]{1,0:T(8,128)S(1)}, f32[16,256]{1,0:T(8,128)S(1)}, u32[]{:S(2)}, u32[]{:S(2)}) collective-permute-start(f32[16,256]{1,0:T(8,128)S(1)} %shard_map.124.refs_0_), channel_id=1, source_target_pairs={{0,3},{1,2},{2,1},{3,0},{4,7},{5,6},{6,5},{7,4},{8,11},{9,10},{10,... | collective-permute-start | bytes 49160 | tf_op jit(solution)/shard_map/ppermute | solution.py:33
  135.7 4.7 %collective-permute-start.59 = (f32[16,256]{1,0:T(8,128)S(1)}, f32[16,256]{1,0:T(8,128)S(1)}, u32[]{:S(2)}, u32[]{:S(2)}) collective-permute-start(f32[16,256]{1,0:T(8,128)S(1)} %shard_map.124.refs_0_), channel_id=1, source_target_pairs={{0,2},{1,3},{2,0},{3,1},{4,6},{5,7},{6,4},{7,5},{8,10},{9,11},{10,... | collective-permute-start | bytes 49160 | tf_op jit(solution)/shard_map/ppermute | solution.py:33
  136.5 3.9 %collective-permute-start.58 = (f32[16,256]{1,0:T(8,128)S(1)}, f32[16,256]{1,0:T(8,128)S(1)}, u32[]{:S(2)}, u32[]{:S(2)}) collective-permute-start(f32[16,256]{1,0:T(8,128)S(1)} %shard_map.124.refs_0_), channel_id=1, source_target_pairs={{0,1},{1,0},{2,3},{3,2},{4,5},{5,4},{6,7},{7,6},{8,9},{9,8},{10,11... | collective-permute-start | bytes 49160 | tf_op jit(solution)/shard_map/ppermute | solution.py:33
  (20 other events, 174.6 us)

commit v13 on v12

--- a/solution.py
+++ b/solution.py
@@ -73,6 +73,8 @@
 
 VMEM = pl.BlockSpec(memory_space=pltpu.VMEM)
 SMEM = pl.BlockSpec(memory_space=pltpu.SMEM)
+HBM = pl.BlockSpec(memory_space=pltpu.HBM)
+ANY = pl.BlockSpec(memory_space=pl.ANY)
 
 
 def local_kernel(body, outs, operands, specs=None, flops=0, scratch=(), limit=None):
@@ -103,8 +105,10 @@
             x, y, (((1,), (1,)), ((), ())), preferred_element_type=jnp.float32
         )
 
+    count = left.shape[0]
     left_top, left_rest = high_low(left)
-    return dot(left_top, top) + (dot(left_top, rest) + dot(left_rest, top))
+    both = dot(jnp.concatenate([left_top, left_rest], axis=0), top)
+    return both[:count] + (dot(left_top, rest) + both[count:])
 
 
 def leaf_shape():
@@ -190,29 +194,26 @@
     )
 
 
-def turn(rhs, first, last, streams):
+def turn(rhs, index, streams, after=None):
     rows, count = rhs.shape[2:]
     depth = count // streams
+    extra = [] if after is None else [after]
 
     def body(rhs_ref, *refs):
-        outs, (held, sem) = refs[:-2], refs[-2:]
-        copy = pltpu.make_async_copy(rhs_ref.at[0, first:last], held, sem)
+        outs, (held, sem) = refs[len(extra) : -2], refs[-2:]
+        copy = pltpu.make_async_copy(rhs_ref.at[0, index], held, sem)
         copy.start()
         copy.wait()
-        for index in range(last - first):
-            wide = jnp.transpose(held[index])
-            for i in range(streams):
-                outs[index * streams + i][...] = wide[i * depth : (i + 1) * depth]
-
-    return local_kernel(
-        body,
-        [float_array(depth, rows)] * (streams * (last - first)),
-        [rhs],
-        [pl.BlockSpec(memory_space=pl.ANY)],
-        scratch=[
-            pltpu.VMEM((last - first, rows, count), jnp.float32),
-            pltpu.SemaphoreType.DMA(()),
-        ],
+        wide = jnp.transpose(held[...])
+        for i in range(streams):
+            outs[i][...] = wide[i * depth : (i + 1) * depth]
+
+    return local_kernel(
+        body,
+        [float_array(depth, rows)] * streams,
+        [rhs, *extra],
+        [HBM] + [ANY] * len(extra),
+        scratch=[pltpu.VMEM((rows, count), jnp.float32), pltpu.SemaphoreType.DMA(())],
     )
 
 
@@ -234,7 +235,7 @@
         body,
         [float_array(1, len(solved), rows, depth * streams), float_array(8, 128)],
         [*flat, after],
-        [VMEM] * len(flat) + [pl.BlockSpec(memory_space=pl.ANY)],
+        [VMEM] * len(flat) + [ANY],
     )
 
 
@@ -302,7 +303,7 @@
         body,
         [float_array(part, width)] * members,
         [*received, rhs_turned, after],
-        [VMEM] * (len(received) + 1) + [pl.BlockSpec(memory_space=pl.ANY)],
+        [VMEM] * (len(received) + 1) + [ANY],
         scratch=[pltpu.VMEM((part, ancestors * order), jnp.float32)],
     )
 
@@ -323,7 +324,7 @@
         body,
         outs,
         [*factors, after],
-        [VMEM] * count + [pl.BlockSpec(memory_space=pl.ANY)],
+        [VMEM] * count + [ANY],
         flops=4 * sum(f.size for f in factors),
     )
 
@@ -380,7 +381,7 @@
         body,
         [float_array(depth, rows)],
         [*held, factor],
-        [VMEM] * members + [pl.BlockSpec(memory_space=pl.ANY)],
+        [VMEM] * members + [HBM],
         flops=6 * depth * rows * order,
         scratch=[
             pltpu.VMEM((depth, order), jnp.float32),
@@ -391,24 +392,30 @@
     )[0]
 
 
-def apply_split(pieces, top, rest, index, base=None, begin=0):
+def apply_split(pieces, top, rest, index, base=None, begin=0, others=None):
     members = lax.axis_size("grp")
     part, width = pieces[0].shape
     rows, order = top.shape[1:]
-    extra = [] if base is None else [base]
+    extra = list(others or []) if base is None else [base]
 
     def body(*refs):
         top_ref, rest_ref = refs[members : members + 2]
         out, whole = refs[-2:]
         put_in_order([refs[d][...] for d in range(members)], whole)
         result = split_product(whole[...], top_ref[index], rest_ref[index])
-        if extra:
+        if others is not None:
+            for i in range(len(others)):
+                out[i] = refs[members + 2 + i][...]
+            out[len(others)] = result
+            return
+        if base is not None:
             result = refs[members + 2][:, begin : begin + rows] - result
         out[...] = result
 
-    return local_kernel(
-        body,
-        [float_array(part, rows)],
+    shape = (part, rows) if others is None else (len(others) + 1, part, rows)
+    return local_kernel(
+        body,
+        [float_array(*shape)],
         [*pieces, top, rest, *extra],
         flops=6 * part * rows * order,
         scratch=[pltpu.VMEM((part, order), jnp.float32)],
@@ -434,8 +441,7 @@
     slots, tile_rows = tiles.shape[2:4]
 
     streams = 2 if rhs_count % 16 == 0 else 1
-    residuals = turn(rhs_local, 0, 1, streams)
-    later = turn(rhs_local, 1, supernodes, streams)
+    residuals = turn(rhs_local, 0, streams)
     solved = []
     gathered = []
     for current in range(supernodes):
@@ -450,8 +456,9 @@
         held = [gather_rows(value) for value in owned]
         gathered.append([assemble(pieces, order) for pieces in held])
         if current + 1 < supernodes:
+            turned = turn(rhs_local, current + 1, streams, owned[0])
             residuals = [
-                later[current * streams + i] - apply_pieces(sub_local, current, pieces)
+                turned[i] - apply_pieces(sub_local, current, pieces)
                 for i, pieces in enumerate(held)
             ]
 
@@ -469,14 +476,18 @@
     )
     solution, left = solve_first(payloads, inverse_top, inverse_rest)
     solutions = [solution]
-    for ancestor in range(1, rhs_anc.shape[0]):
+    ancestors = rhs_anc.shape[0]
+    for ancestor in range(1, ancestors):
         pieces = [piece for _, piece in gather_rows(solutions[-1])]
         residual = apply_split(
             pieces, below_top, below_rest, ancestor - 1, left, (ancestor - 1) * rows
         )
         pieces = [piece for _, piece in gather_rows(residual)]
-        solutions.append(apply_split(pieces, inverse_top, inverse_rest, ancestor))
-    solutions = jnp.swapaxes(jnp.stack(solutions), 1, 2)
+        others = solutions if ancestor + 1 == ancestors else None
+        solved_now = apply_split(pieces, inverse_top, inverse_rest, ancestor, others=others)
+        solutions.append(solved_now)
+    solutions = solutions[-1] if ancestors > 1 else solutions[0][None]
+    solutions = jnp.swapaxes(solutions, 1, 2)
     return (solution_local, solutions)
 
 

time: 142 us -> 154 us (1.085)
  waiting for transfers between devices: 16.5 us -> 37.7 us
  local copies, waits for them, and re-layouts: 8.63 us -> 3.88 us
  starting transfers between devices: 90.3 us -> 86.8 us
    ppermute x57, waiting for transfers between devices: 11.4 us -> 32.6 us  [send(): return lax.ppermute(value, axis, pairs)]
    unnamed x46 -> x22, local copies, waits for them, and re-layouts: 8.19 us -> 3.43 us
    ppermute x57, starting transfers between devices: 86.7 us -> 83.2 us  [send(): return lax.ppermute(value, axis, pairs)]
    pallas_call x13 -> x15, Pallas kernels: 9.44 us -> 9.38 us  [local_kernel(): pl.pallas_call(body, out_shape=list(outs), in_specs=specs or [VMEM] * len...]
  transfers between devices with their start and end apart: 61 -> 61, of which waited for: 12 -> 17; matrix products, arithmetic and copies ran while one was open for 10% -> 9% of each run, Pallas kernels for 4% -> 4%
where the time goes in v13:
time: 154 us
  starting transfers between devices  86.8 us (56%)
  waiting for transfers between devices  37.7 us (24%)
  matrix products  13.6 us (9%)
  Pallas kernels  9.38 us (6%)
  local copies, waits for them, and re-layouts  3.88 us (3%)
  between operations  2.43 us (2%)
    ppermute x57, starting transfers between devices, send(): return lax.ppermute(value, axis, pairs)  83.2 us
    ppermute x57, waiting for transfers between devices, send(): return lax.ppermute(value, axis, pairs)  32.6 us
    dot_general x48, matrix products, contract_last(): lax.dot_general(left, right, (((left.ndim - 1,), (right.ndim - 1,)), ((),...  13.6 us
    pallas_call x15, Pallas kernels, local_kernel(): pl.pallas_call(body, out_shape=list(outs), in_specs=specs or [VMEM] * len...  9.38 us
    ppermute x3, waiting for transfers between devices, swap(): return lax.ppermute(value, axis, pairs)  3.7 us
    ppermute x3, starting transfers between devices, swap(): return lax.ppermute(value, axis, pairs)  3.55 us
    unnamed x22, local copies, waits for them, and re-layouts  3.43 us
  transfers between devices with their start and end apart: 61, of which 17 were waited for; matrix products, arithmetic and copies ran while one was open for 9% of the time, Pallas kernels for 4%

profile of v13, /device:TPU:0, one launch (start us, length us, event | category | flops | bytes accessed | tf_op | source)
XLA Modules:
  0.0 153.9 jit_solution(8414442422907646584)
XLA Ops:
  0.7 1.2 copy-done.3
  2.1 5.1 %collective-permute-start.2 = (f32[64,256]{1,0:T(8,128)S(1)}, f32[64,256]{1,0:T(8,128)S(1)}, u32[]{:S(2)}, u32[]{:S(2)}) collective-permute-start(f32[64,256]{1,0:T(8,128)S(1)} %get-tuple-element.28.refs_0_), channel_id=1, source_target_pairs={{0,3},{1,2},{2,1},{3,0},{4,7},{5,6},{6,5},{7,4},{8,11},{9,10},{10,... | collective-permute-start | bytes 196616 | tf_op jit(solution)/shard_map/ppermute | solution.py:33
  7.2 0.6 collective-permute-start
  7.8 3.7 %collective-permute-start.5 = (f32[64,256]{1,0:T(8,128)S(1)}, f32[64,256]{1,0:T(8,128)S(1)}, u32[]{:S(2)}, u32[]{:S(2)}) collective-permute-start(f32[64,256]{1,0:T(8,128)S(1)} %get-tuple-element.29.refs_0_), channel_id=1, source_target_pairs={{0,3},{1,2},{2,1},{3,0},{4,7},{5,6},{6,5},{7,4},{8,11},{9,10},{10,... | collective-permute-start | bytes 196616 | tf_op jit(solution)/shard_map/ppermute | solution.py:33
  11.6 0.8 collective-permute-start.3
  13.1 2.8 %collective-permute-done.1.refs_2_ = f32[64,256]{1,0:T(8,128)} collective-permute-done((f32[64,256]{1,0:T(8,128)S(1)}, f32[64,256]{1,0:T(8,128)}, u32[]{:S(2)}, u32[]{:S(2)}) %collective-permute-start.1) | collective-permute-done | bytes 65568 | tf_op jit(solution)/shard_map/ppermute | solution.py:33
  15.9 2.2 %copy-done.1 = f32[1,4,256,1024]{3,2,1,0:T(8,128)S(1)} copy-done((f32[1,4,256,1024]{3,2,1,0:T(8,128)S(1)}, f32[1,4,256,1024]{3,2,1,0:T(8,128)}, u32[]{:S(2)}) %copy-start.1) | copy-done | bytes 4194328
  18.1 1.6 %shard_map.114.refs_0_ = f32[64,256]{1,0:T(8,128)S(1)} custom-call(f32[64,256]{1,0:T(8,128)S(1)} %get-tuple-element.28.refs_0_, f32[64,256]{1,0:T(8,128)} %collective-permute-done.refs_1_, f32[64,256]{1,0:T(8,128)} %collective-permute-done.1.refs_2_, f32[64,256]{1,0:T(8,128)S(1)} %collective-permute-done.2.refs_3_, f32[1,4,256,1024]{3,2,1,0:T(8,128)S(1)} %copy-done.1), custom_call_target="tpu_custom_call" | custom-call | flops 100663296 | bytes 4521984 | tf_op jit(solution)/shard_map/pallas_call | solution.py:82
  19.7 2.6 %collective-permute-start.8 = (f32[64,256]{1,0:T(8,128)S(1)}, f32[64,256]{1,0:T(8,128)S(1)}, u32[]{:S(2)}, u32[]{:S(2)}) collective-permute-start(f32[64,256]{1,0:T(8,128)S(1)} %shard_map.114.refs_0_), channel_id=1, source_target_pairs={{0,3},{1,2},{2,1},{3,0},{4,7},{5,6},{6,5},{7,4},{8,11},{9,10},{10,... | collective-permute-start | bytes 196616 | tf_op jit(solution)/shard_map/ppermute | solution.py:33
  22.3 1.8 %collective-permute-start.6 = (f32[64,256]{1,0:T(8,128)S(1)}, f32[64,256]{1,0:T(8,128)S(1)}, u32[]{:S(2)}, u32[]{:S(2)}) collective-permute-start(f32[64,256]{1,0:T(8,128)S(1)} %shard_map.114.refs_0_), channel_id=1, source_target_pairs={{0,1},{1,0},{2,3},{3,2},{4,5},{5,4},{6,7},{7,6},{8,9},{9,8},{10,11... | collective-permute-start | bytes 196616 | tf_op jit(solution)/shard_map/ppermute | solution.py:33
  24.2 0.6 shard_map.115.refs_1_
  24.8 2.6 %collective-permute-start.14 = (f32[64,256]{1,0:T(8,128)S(1)}, f32[64,256]{1,0:T(8,128)S(1)}, u32[]{:S(2)}, u32[]{:S(2)}) collective-permute-start(f32[64,256]{1,0:T(8,128)S(1)} %shard_map.115.refs_1_), channel_id=1, source_target_pairs={{0,3},{1,2},{2,1},{3,0},{4,7},{5,6},{6,5},{7,4},{8,11},{9,10},{10,... | collective-permute-start | bytes 196616 | tf_op jit(solution)/shard_map/ppermute | solution.py:33
  27.8 3.3 %collective-permute-done.14 = f32[64,256]{1,0:T(8,128)S(1)} collective-permute-done((f32[64,256]{1,0:T(8,128)S(1)}, f32[64,256]{1,0:T(8,128)S(1)}, u32[]{:S(2)}, u32[]{:S(2)}) %collective-permute-start.14) | collective-permute-done | bytes 65568 | tf_op jit(solution)/shard_map/ppermute | solution.py:33
  31.1 1.2 collective-permute-start.12
  32.9 2.5 %collective-permute-done.12 = f32[64,256]{1,0:T(8,128)S(1)} collective-permute-done((f32[64,256]{1,0:T(8,128)S(1)}, f32[64,256]{1,0:T(8,128)S(1)}, u32[]{:S(2)}, u32[]{:S(2)}) %collective-permute-start.12) | collective-permute-done | bytes 65568 | tf_op jit(solution)/shard_map/ppermute | solution.py:33
  35.9 4.0 %collective-permute-start.17 = (f32[64,256]{1,0:T(8,128)S(1)}, f32[64,256]{1,0:T(8,128)S(1)}, u32[]{:S(2)}, u32[]{:S(2)}) collective-permute-start(f32[64,256]{1,0:T(8,128)S(1)} %sub.19), channel_id=1, source_target_pairs={{0,3},{1,2},{2,1},{3,0},{4,7},{5,6},{6,5},{7,4},{8,11},{9,10},{10,... | collective-permute-start | bytes 196616 | tf_op jit(solution)/shard_map/ppermute | solution.py:33
  39.9 0.6 collective-permute-start.15
  41.8 3.8 %collective-permute-start.11 = (f32[64,256]{1,0:T(8,128)S(1)}, f32[64,256]{1,0:T(8,128)S(1)}, u32[]{:S(2)}, u32[]{:S(2)}) collective-permute-start(f32[64,256]{1,0:T(8,128)S(1)} %sub.18), channel_id=1, source_target_pairs={{0,3},{1,2},{2,1},{3,0},{4,7},{5,6},{6,5},{7,4},{8,11},{9,10},{10,... | collective-permute-start | bytes 196616 | tf_op jit(solution)/shard_map/ppermute | solution.py:33
  45.7 0.8 collective-permute-start.9
  48.0 3.7 %collective-permute-start.26 = (f32[64,256]{1,0:T(8,128)S(1)}, f32[64,256]{1,0:T(8,128)S(1)}, u32[]{:S(2)}, u32[]{:S(2)}) collective-permute-start(f32[64,256]{1,0:T(8,128)S(1)} %get-tuple-element.61.refs_3_), channel_id=1, source_target_pairs={{0,3},{1,2},{2,1},{3,0},{4,7},{5,6},{6,5},{7,4},{8,11},{9,10},{10,... | collective-permute-start | bytes 196616 | tf_op jit(solution)/shard_map/ppermute | solution.py:33
  51.7 0.8 collective-permute-start.24
  54.0 3.7 %collective-permute-start.20 = (f32[64,256]{1,0:T(8,128)S(1)}, f32[64,256]{1,0:T(8,128)S(1)}, u32[]{:S(2)}, u32[]{:S(2)}) collective-permute-start(f32[64,256]{1,0:T(8,128)S(1)} %get-tuple-element.55.refs_0_.refs_2_), channel_id=1, source_target_pairs={{0,3},{1,2},{2,1},{3,0},{4,7},{5,6},{6,5},{7,4},{8,11},{9,10},{10,... | collective-permute-start | bytes 196616 | tf_op jit(solution)/shard_map/ppermute | solution.py:33
  58.0 1.1 collective-permute-start.18
  60.2 3.4 %collective-permute-start.29 = (f32[64,256]{1,0:T(8,128)S(1)}, f32[64,256]{1,0:T(8,128)S(1)}, u32[]{:S(2)}, u32[]{:S(2)}) collective-permute-start(f32[64,256]{1,0:T(8,128)S(1)} %sub.21), channel_id=1, source_target_pairs={{0,3},{1,2},{2,1},{3,0},{4,7},{5,6},{6,5},{7,4},{8,11},{9,10},{10,... | collective-permute-start | bytes 196616 | tf_op jit(solution)/shard_map/ppermute | solution.py:33
  63.9 0.8 collective-permute-start.27
  65.9 3.4 %collective-permute-start.23 = (f32[64,256]{1,0:T(8,128)S(1)}, f32[64,256]{1,0:T(8,128)S(1)}, u32[]{:S(2)}, u32[]{:S(2)}) collective-permute-start(f32[64,256]{1,0:T(8,128)S(1)} %sub.20), channel_id=1, source_target_pairs={{0,3},{1,2},{2,1},{3,0},{4,7},{5,6},{6,5},{7,4},{8,11},{9,10},{10,... | collective-permute-start | bytes 196616 | tf_op jit(solution)/shard_map/ppermute | solution.py:33
  69.5 1.1 collective-permute-start.21
  71.8 3.4 %collective-permute-start.38 = (f32[64,256]{1,0:T(8,128)S(1)}, f32[64,256]{1,0:T(8,128)S(1)}, u32[]{:S(2)}, u32[]{:S(2)}) collective-permute-start(f32[64,256]{1,0:T(8,128)S(1)} %get-tuple-element.63.refs_5_), channel_id=1, source_target_pairs={{0,3},{1,2},{2,1},{3,0},{4,7},{5,6},{6,5},{7,4},{8,11},{9,10},{10,... | collective-permute-start | bytes 196616 | tf_op jit(solution)/shard_map/ppermute | solution.py:33
  75.2 1.0 collective-permute-start.36
  77.4 3.4 %collective-permute-start.32 = (f32[64,256]{1,0:T(8,128)S(1)}, f32[64,256]{1,0:T(8,128)S(1)}, u32[]{:S(2)}, u32[]{:S(2)}) collective-permute-start(f32[64,256]{1,0:T(8,128)S(1)} %get-tuple-element.57.refs_0_.refs_4_), channel_id=1, source_target_pairs={{0,3},{1,2},{2,1},{3,0},{4,7},{5,6},{6,5},{7,4},{8,11},{9,10},{10,... | collective-permute-start | bytes 196616 | tf_op jit(solution)/shard_map/ppermute | solution.py:33
  81.4 1.1 collective-permute-start.30
  83.6 3.4 %collective-permute-start.41 = (f32[64,256]{1,0:T(8,128)S(1)}, f32[64,256]{1,0:T(8,128)S(1)}, u32[]{:S(2)}, u32[]{:S(2)}) collective-permute-start(f32[64,256]{1,0:T(8,128)S(1)} %sub.23), channel_id=1, source_target_pairs={{0,3},{1,2},{2,1},{3,0},{4,7},{5,6},{6,5},{7,4},{8,11},{9,10},{10,... | collective-permute-start | bytes 196616 | tf_op jit(solution)/shard_map/ppermute | solution.py:33
  87.1 1.0 collective-permute-start.39
  89.3 3.4 %collective-permute-start.35 = (f32[64,256]{1,0:T(8,128)S(1)}, f32[64,256]{1,0:T(8,128)S(1)}, u32[]{:S(2)}, u32[]{:S(2)}) collective-permute-start(f32[64,256]{1,0:T(8,128)S(1)} %sub.22), channel_id=1, source_target_pairs={{0,3},{1,2},{2,1},{3,0},{4,7},{5,6},{6,5},{7,4},{8,11},{9,10},{10,... | collective-permute-start | bytes 196616 | tf_op jit(solution)/shard_map/ppermute | solution.py:33
  92.9 5.2 %collective-permute-done.33 = f32[64,256]{1,0:T(8,128)S(1)} collective-permute-done((f32[64,256]{1,0:T(8,128)S(1)}, f32[64,256]{1,0:T(8,128)S(1)}, u32[]{:S(2)}, u32[]{:S(2)}) %collective-permute-start.33) | collective-permute-done | bytes 65568 | tf_op jit(solution)/shard_map/ppermute | solution.py:33
  98.7 5.2 %collective-permute-done.34 = f32[64,256]{1,0:T(8,128)S(1)} collective-permute-done((f32[64,256]{1,0:T(8,128)S(1)}, f32[64,256]{1,0:T(8,128)S(1)}, u32[]{:S(2)}, u32[]{:S(2)}) %collective-permute-start.34) | collective-permute-done | bytes 65568 | tf_op jit(solution)/shard_map/ppermute | solution.py:33
  105.5 0.8 collective-permute-start.47
  106.3 2.4 %collective-permute-start.46 = (f32[64,256]{1,0:T(8,128)S(1)}, f32[64,256]{1,0:T(8,128)S(1)}, u32[]{:S(2)}, u32[]{:S(2)}) collective-permute-start(f32[64,256]{1,0:T(8,128)S(1)} %get-tuple-element.65.refs_7_), channel_id=1, source_target_pairs={{0,2},{1,3},{2,0},{3,1},{4,6},{5,7},{6,4},{7,5},{8,10},{9,11},{10,... | collective-permute-start | bytes 196616 | tf_op jit(solution)/shard_map/ppermute | solution.py:33
  108.8 1.2 collective-permute-start.45
  110.0 0.7 collective-permute-start.44
  110.7 1.6 %collective-permute-start.43 = (f32[64,256]{1,0:T(8,128)S(1)}, f32[64,256]{1,0:T(8,128)S(1)}, u32[]{:S(2)}, u32[]{:S(2)}) collective-permute-start(f32[64,256]{1,0:T(8,128)S(1)} %get-tuple-element.59.refs_6_), channel_id=1, source_target_pairs={{0,2},{1,3},{2,0},{3,1},{4,6},{5,7},{6,4},{7,5},{8,10},{9,11},{10,... | collective-permute-start | bytes 196616 | tf_op jit(solution)/shard_map/ppermute | solution.py:33
  112.3 5.0 %collective-permute-done.43 = f32[64,256]{1,0:T(8,128)S(1)} collective-permute-done((f32[64,256]{1,0:T(8,128)S(1)}, f32[64,256]{1,0:T(8,128)S(1)}, u32[]{:S(2)}, u32[]{:S(2)}) %collective-permute-start.43) | collective-permute-done | bytes 65568 | tf_op jit(solution)/shard_map/ppermute | solution.py:33
  117.4 1.2 shard_map.119.refs_0_
  118.7 1.2 shard_map.120
  120.0 1.3 collective-permute-done.48.refs_1_
  121.3 1.6 %collective-permute-start.49 = (f32[2,16,512]{2,1,0:T(8,128)S(1)}, f32[2,16,512]{2,1,0:T(8,128)S(1)}, u32[]{:S(2)}, u32[]{:S(2)}) collective-permute-start(f32[2,16,512]{2,1,0:T(8,128)S(1)} %get-tuple-element.40), channel_id=1, source_target_pairs={{0,8},{4,12},{8,0},{12,4},{16,24},{20,28},{24,16},{28,20},{1,9},{5... | collective-permute-start | bytes 196616 | tf_op jit(solution)/shard_map/ppermute | solution.py:71
  122.9 1.5 collective-permute-start.50
  124.9 1.0 shard_map.121
  125.9 1.3 collective-permute-done.50.refs_2_
  127.2 2.4 %collective-permute-done.51.refs_3_ = f32[2,16,512]{2,1,0:T(8,128)S(1)} collective-permute-done((f32[2,16,512]{2,1,0:T(8,128)S(1)}, f32[2,16,512]{2,1,0:T(8,128)S(1)}, u32[]{:S(2)}, u32[]{:S(2)}) %collective-permute-start.51) | collective-permute-done | bytes 65568 | tf_op jit(solution)/shard_map/ppermute | solution.py:71
  130.2 2.2 %collective-permute-start.53 = (f32[16,1280]{1,0:T(8,128)S(1)}, f32[16,1280]{1,0:T(8,128)S(1)}, u32[]{:S(2)}, u32[]{:S(2)}) collective-permute-start(f32[16,1280]{1,0:T(8,128)S(1)} %get-tuple-element.46), channel_id=1, source_target_pairs={{0,2},{1,3},{2,0},{3,1},{4,6},{5,7},{6,4},{7,5},{8,10},{9,11},{10,... | collective-permute-start | bytes 245768 | tf_op jit(solution)/shard_map/ppermute | solution.py:33
  132.4 2.1 %collective-permute-start.54 = (f32[16,1280]{1,0:T(8,128)S(1)}, f32[16,1280]{1,0:T(8,128)S(1)}, u32[]{:S(2)}, u32[]{:S(2)}) collective-permute-start(f32[16,1280]{1,0:T(8,128)S(1)} %get-tuple-element.47), channel_id=1, source_target_pairs={{0,3},{1,2},{2,1},{3,0},{4,7},{5,6},{6,5},{7,4},{8,11},{9,10},{10,... | collective-permute-start | bytes 245768 | tf_op jit(solution)/shard_map/ppermute | solution.py:33
  134.9 2.4 %collective-permute-done.53.refs_2_ = f32[16,1280]{1,0:T(8,128)S(1)} collective-permute-done((f32[16,1280]{1,0:T(8,128)S(1)}, f32[16,1280]{1,0:T(8,128)S(1)}, u32[]{:S(2)}, u32[]{:S(2)}) %collective-permute-start.53) | collective-permute-done | bytes 81952 | tf_op jit(solution)/shard_map/ppermute | solution.py:33
  137.3 1.4 collective-permute-done.54.refs_3_
  139.1 2.1 %collective-permute-start.57 = (f32[16,256]{1,0:T(8,128)S(1)}, f32[16,256]{1,0:T(8,128)S(1)}, u32[]{:S(2)}, u32[]{:S(2)}) collective-permute-start(f32[16,256]{1,0:T(8,128)S(1)} %get-tuple-element.50.refs_0_.refs_6_), channel_id=1, source_target_pairs={{0,3},{1,2},{2,1},{3,0},{4,7},{5,6},{6,5},{7,4},{8,11},{9,10},{10,... | collective-permute-start | bytes 49160 | tf_op jit(solution)/shard_map/ppermute | solution.py:33
  141.7 1.8 %collective-permute-start.55 = (f32[16,256]{1,0:T(8,128)S(1)}, f32[16,256]{1,0:T(8,128)S(1)}, u32[]{:S(2)}, u32[]{:S(2)}) collective-permute-start(f32[16,256]{1,0:T(8,128)S(1)} %get-tuple-element.50.refs_0_.refs_6_), channel_id=1, source_target_pairs={{0,1},{1,0},{2,3},{3,2},{4,5},{5,4},{6,7},{7,6},{8,9},{9,8},{10,11... | collective-permute-start | bytes 49160 | tf_op jit(solution)/shard_map/ppermute | solution.py:33
  143.5 1.1 collective-permute-done.57.refs_3_
  144.7 1.2 collective-permute-done.56.refs_2_
  146.2 1.8 %collective-permute-start.60 = (f32[16,256]{1,0:T(8,128)S(1)}, f32[16,256]{1,0:T(8,128)S(1)}, u32[]{:S(2)}, u32[]{:S(2)}) collective-permute-start(f32[16,256]{1,0:T(8,128)S(1)} %shard_map.126.refs_0_), channel_id=1, source_target_pairs={{0,3},{1,2},{2,1},{3,0},{4,7},{5,6},{6,5},{7,4},{8,11},{9,10},{10,... | collective-permute-start | bytes 49160 | tf_op jit(solution)/shard_map/ppermute | solution.py:33
  148.0 1.1 collective-permute-start.59
  149.1 1.5 collective-permute-start.58
  150.6 1.1 collective-permute-done.60.refs_3_
  151.8 0.9 collective-permute-done.59.refs_2_
  152.9 1.0 shard_map.127
  (183 shorter events, 19.3 us)
Async XLA Ops:
  0.6 31.7 %copy-start = (f32[1,3,256,1024]{3,2,1,0:T(8,128)S(1)}, f32[1,3,256,1024]{3,2,1,0:T(8,128)}, u32[]{:S(2)}) copy-start(f32[1,3,256,1024]{3,2,1,0:T(8,128)} %param.12) | copy-start | bytes 9437188
  2.1 9.5 %collective-permute-start.2 = (f32[64,256]{1,0:T(8,128)S(1)}, f32[64,256]{1,0:T(8,128)S(1)}, u32[]{:S(2)}, u32[]{:S(2)}) collective-permute-start(f32[64,256]{1,0:T(8,128)S(1)} %get-tuple-element.28.refs_0_), channel_id=1, source_target_pairs={{0,3},{1,2},{2,1},{3,0},{4,7},{5,6},{6,5},{7,4},{8,11},{9,10},{10,... | collective-permute-start | bytes 196616 | tf_op jit(solution)/shard_map/ppermute | solution.py:33
  7.2 8.7 %collective-permute-start.1 = (f32[64,256]{1,0:T(8,128)S(1)}, f32[64,256]{1,0:T(8,128)}, u32[]{:S(2)}, u32[]{:S(2)}) collective-permute-start(f32[64,256]{1,0:T(8,128)S(1)} %get-tuple-element.28.refs_0_), channel_id=1, source_target_pairs={{0,2},{1,3},{2,0},{3,1},{4,6},{5,7},{6,4},{7,5},{8,10},{9,11},{10,... | collective-permute-start | bytes 196616 | tf_op jit(solution)/shard_map/ppermute | solution.py:33
  7.2 8.7 %collective-permute-start = (f32[64,256]{1,0:T(8,128)S(1)}, f32[64,256]{1,0:T(8,128)}, u32[]{:S(2)}, u32[]{:S(2)}) collective-permute-start(f32[64,256]{1,0:T(8,128)S(1)} %get-tuple-element.28.refs_0_), channel_id=1, source_target_pairs={{0,1},{1,0},{2,3},{3,2},{4,5},{5,4},{6,7},{7,6},{8,9},{9,8},{10,11... | collective-permute-start | bytes 196616 | tf_op jit(solution)/shard_map/ppermute | solution.py:33
  7.8 14.5 %collective-permute-start.5 = (f32[64,256]{1,0:T(8,128)S(1)}, f32[64,256]{1,0:T(8,128)S(1)}, u32[]{:S(2)}, u32[]{:S(2)}) collective-permute-start(f32[64,256]{1,0:T(8,128)S(1)} %get-tuple-element.29.refs_0_), channel_id=1, source_target_pairs={{0,3},{1,2},{2,1},{3,0},{4,7},{5,6},{6,5},{7,4},{8,11},{9,10},{10,... | collective-permute-start | bytes 196616 | tf_op jit(solution)/shard_map/ppermute | solution.py:33
  11.6 12.6 %collective-permute-start.4 = (f32[64,256]{1,0:T(8,128)S(1)}, f32[64,256]{1,0:T(8,128)S(1)}, u32[]{:S(2)}, u32[]{:S(2)}) collective-permute-start(f32[64,256]{1,0:T(8,128)S(1)} %get-tuple-element.29.refs_0_), channel_id=1, source_target_pairs={{0,2},{1,3},{2,0},{3,1},{4,6},{5,7},{6,4},{7,5},{8,10},{9,11},{10,... | collective-permute-start | bytes 196616 | tf_op jit(solution)/shard_map/ppermute | solution.py:33
  11.6 12.6 %collective-permute-start.3 = (f32[64,256]{1,0:T(8,128)S(1)}, f32[64,256]{1,0:T(8,128)S(1)}, u32[]{:S(2)}, u32[]{:S(2)}) collective-permute-start(f32[64,256]{1,0:T(8,128)S(1)} %get-tuple-element.29.refs_0_), channel_id=1, source_target_pairs={{0,1},{1,0},{2,3},{3,2},{4,5},{5,4},{6,7},{7,6},{8,9},{9,8},{10,11... | collective-permute-start | bytes 196616 | tf_op jit(solution)/shard_map/ppermute | solution.py:33
  19.7 20.2 %collective-permute-start.8 = (f32[64,256]{1,0:T(8,128)S(1)}, f32[64,256]{1,0:T(8,128)S(1)}, u32[]{:S(2)}, u32[]{:S(2)}) collective-permute-start(f32[64,256]{1,0:T(8,128)S(1)} %shard_map.114.refs_0_), channel_id=1, source_target_pairs={{0,3},{1,2},{2,1},{3,0},{4,7},{5,6},{6,5},{7,4},{8,11},{9,10},{10,... | collective-permute-start | bytes 196616 | tf_op jit(solution)/shard_map/ppermute | solution.py:33
  22.3 18.5 %collective-permute-start.7 = (f32[64,256]{1,0:T(8,128)S(1)}, f32[64,256]{1,0:T(8,128)S(1)}, u32[]{:S(2)}, u32[]{:S(2)}) collective-permute-start(f32[64,256]{1,0:T(8,128)S(1)} %shard_map.114.refs_0_), channel_id=1, source_target_pairs={{0,2},{1,3},{2,0},{3,1},{4,6},{5,7},{6,4},{7,5},{8,10},{9,11},{10,... | collective-permute-start | bytes 196616 | tf_op jit(solution)/shard_map/ppermute | solution.py:33
  22.3 18.8 %collective-permute-start.6 = (f32[64,256]{1,0:T(8,128)S(1)}, f32[64,256]{1,0:T(8,128)S(1)}, u32[]{:S(2)}, u32[]{:S(2)}) collective-permute-start(f32[64,256]{1,0:T(8,128)S(1)} %shard_map.114.refs_0_), channel_id=1, source_target_pairs={{0,1},{1,0},{2,3},{3,2},{4,5},{5,4},{6,7},{7,6},{8,9},{9,8},{10,11... | collective-permute-start | bytes 196616 | tf_op jit(solution)/shard_map/ppermute | solution.py:33
  24.8 6.3 %collective-permute-start.14 = (f32[64,256]{1,0:T(8,128)S(1)}, f32[64,256]{1,0:T(8,128)S(1)}, u32[]{:S(2)}, u32[]{:S(2)}) collective-permute-start(f32[64,256]{1,0:T(8,128)S(1)} %shard_map.115.refs_1_), channel_id=1, source_target_pairs={{0,3},{1,2},{2,1},{3,0},{4,7},{5,6},{6,5},{7,4},{8,11},{9,10},{10,... | collective-permute-start | bytes 196616 | tf_op jit(solution)/shard_map/ppermute | solution.py:33
  27.4 5.2 %collective-permute-start.13 = (f32[64,256]{1,0:T(8,128)S(1)}, f32[64,256]{1,0:T(8,128)S(1)}, u32[]{:S(2)}, u32[]{:S(2)}) collective-permute-start(f32[64,256]{1,0:T(8,128)S(1)} %shard_map.115.refs_1_), channel_id=1, source_target_pairs={{0,2},{1,3},{2,0},{3,1},{4,6},{5,7},{6,4},{7,5},{8,10},{9,11},{10,... | collective-permute-start | bytes 196616 | tf_op jit(solution)/shard_map/ppermute | solution.py:33
  31.1 4.3 %collective-permute-start.12 = (f32[64,256]{1,0:T(8,128)S(1)}, f32[64,256]{1,0:T(8,128)S(1)}, u32[]{:S(2)}, u32[]{:S(2)}) collective-permute-start(f32[64,256]{1,0:T(8,128)S(1)} %shard_map.115.refs_1_), channel_id=1, source_target_pairs={{0,1},{1,0},{2,3},{3,2},{4,5},{5,4},{6,7},{7,6},{8,9},{9,8},{10,11... | collective-permute-start | bytes 196616 | tf_op jit(solution)/shard_map/ppermute | solution.py:33
  35.9 11.2 %collective-permute-start.17 = (f32[64,256]{1,0:T(8,128)S(1)}, f32[64,256]{1,0:T(8,128)S(1)}, u32[]{:S(2)}, u32[]{:S(2)}) collective-permute-start(f32[64,256]{1,0:T(8,128)S(1)} %sub.19), channel_id=1, source_target_pairs={{0,3},{1,2},{2,1},{3,0},{4,7},{5,6},{6,5},{7,4},{8,11},{9,10},{10,... | collective-permute-start | bytes 196616 | tf_op jit(solution)/shard_map/ppermute | solution.py:33
  39.9 7.5 %collective-permute-start.16 = (f32[64,256]{1,0:T(8,128)S(1)}, f32[64,256]{1,0:T(8,128)S(1)}, u32[]{:S(2)}, u32[]{:S(2)}) collective-permute-start(f32[64,256]{1,0:T(8,128)S(1)} %sub.19), channel_id=1, source_target_pairs={{0,2},{1,3},{2,0},{3,1},{4,6},{5,7},{6,4},{7,5},{8,10},{9,11},{10,... | collective-permute-start | bytes 196616 | tf_op jit(solution)/shard_map/ppermute | solution.py:33
  39.9 5.8 %collective-permute-start.15 = (f32[64,256]{1,0:T(8,128)S(1)}, f32[64,256]{1,0:T(8,128)S(1)}, u32[]{:S(2)}, u32[]{:S(2)}) collective-permute-start(f32[64,256]{1,0:T(8,128)S(1)} %sub.19), channel_id=1, source_target_pairs={{0,1},{1,0},{2,3},{3,2},{4,5},{5,4},{6,7},{7,6},{8,9},{9,8},{10,11... | collective-permute-start | bytes 196616 | tf_op jit(solution)/shard_map/ppermute | solution.py:33
  41.8 11.3 %collective-permute-start.11 = (f32[64,256]{1,0:T(8,128)S(1)}, f32[64,256]{1,0:T(8,128)S(1)}, u32[]{:S(2)}, u32[]{:S(2)}) collective-permute-start(f32[64,256]{1,0:T(8,128)S(1)} %sub.18), channel_id=1, source_target_pairs={{0,3},{1,2},{2,1},{3,0},{4,7},{5,6},{6,5},{7,4},{8,11},{9,10},{10,... | collective-permute-start | bytes 196616 | tf_op jit(solution)/shard_map/ppermute | solution.py:33
  45.6 7.8 %collective-permute-start.10 = (f32[64,256]{1,0:T(8,128)S(1)}, f32[64,256]{1,0:T(8,128)S(1)}, u32[]{:S(2)}, u32[]{:S(2)}) collective-permute-start(f32[64,256]{1,0:T(8,128)S(1)} %sub.18), channel_id=1, source_target_pairs={{0,2},{1,3},{2,0},{3,1},{4,6},{5,7},{6,4},{7,5},{8,10},{9,11},{10,... | collective-permute-start | bytes 196616 | tf_op jit(solution)/shard_map/ppermute | solution.py:33
  45.7 6.0 %collective-permute-start.9 = (f32[64,256]{1,0:T(8,128)S(1)}, f32[64,256]{1,0:T(8,128)S(1)}, u32[]{:S(2)}, u32[]{:S(2)}) collective-permute-start(f32[64,256]{1,0:T(8,128)S(1)} %sub.18), channel_id=1, source_target_pairs={{0,1},{1,0},{2,3},{3,2},{4,5},{5,4},{6,7},{7,6},{8,9},{9,8},{10,11... | collective-permute-start | bytes 196616 | tf_op jit(solution)/shard_map/ppermute | solution.py:33
  48.0 11.3 %collective-permute-start.26 = (f32[64,256]{1,0:T(8,128)S(1)}, f32[64,256]{1,0:T(8,128)S(1)}, u32[]{:S(2)}, u32[]{:S(2)}) collective-permute-start(f32[64,256]{1,0:T(8,128)S(1)} %get-tuple-element.61.refs_3_), channel_id=1, source_target_pairs={{0,3},{1,2},{2,1},{3,0},{4,7},{5,6},{6,5},{7,4},{8,11},{9,10},{10,... | collective-permute-start | bytes 196616 | tf_op jit(solution)/shard_map/ppermute | solution.py:33
  51.7 7.9 %collective-permute-start.25 = (f32[64,256]{1,0:T(8,128)S(1)}, f32[64,256]{1,0:T(8,128)S(1)}, u32[]{:S(2)}, u32[]{:S(2)}) collective-permute-start(f32[64,256]{1,0:T(8,128)S(1)} %get-tuple-element.61.refs_3_), channel_id=1, source_target_pairs={{0,2},{1,3},{2,0},{3,1},{4,6},{5,7},{6,4},{7,5},{8,10},{9,11},{10,... | collective-permute-start | bytes 196616 | tf_op jit(solution)/shard_map/ppermute | solution.py:33
  51.7 6.2 %collective-permute-start.24 = (f32[64,256]{1,0:T(8,128)S(1)}, f32[64,256]{1,0:T(8,128)S(1)}, u32[]{:S(2)}, u32[]{:S(2)}) collective-permute-start(f32[64,256]{1,0:T(8,128)S(1)} %get-tuple-element.61.refs_3_), channel_id=1, source_target_pairs={{0,1},{1,0},{2,3},{3,2},{4,5},{5,4},{6,7},{7,6},{8,9},{9,8},{10,11... | collective-permute-start | bytes 196616 | tf_op jit(solution)/shard_map/ppermute | solution.py:33
  54.0 11.0 %collective-permute-start.20 = (f32[64,256]{1,0:T(8,128)S(1)}, f32[64,256]{1,0:T(8,128)S(1)}, u32[]{:S(2)}, u32[]{:S(2)}) collective-permute-start(f32[64,256]{1,0:T(8,128)S(1)} %get-tuple-element.55.refs_0_.refs_2_), channel_id=1, source_target_pairs={{0,3},{1,2},{2,1},{3,0},{4,7},{5,6},{6,5},{7,4},{8,11},{9,10},{10,... | collective-permute-start | bytes 196616 | tf_op jit(solution)/shard_map/ppermute | solution.py:33
  57.7 7.6 %collective-permute-start.19 = (f32[64,256]{1,0:T(8,128)S(1)}, f32[64,256]{1,0:T(8,128)S(1)}, u32[]{:S(2)}, u32[]{:S(2)}) collective-permute-start(f32[64,256]{1,0:T(8,128)S(1)} %get-tuple-element.55.refs_0_.refs_2_), channel_id=1, source_target_pairs={{0,2},{1,3},{2,0},{3,1},{4,6},{5,7},{6,4},{7,5},{8,10},{9,11},{10,... | collective-permute-start | bytes 196616 | tf_op jit(solution)/shard_map/ppermute | solution.py:33
  58.0 5.9 %collective-permute-start.18 = (f32[64,256]{1,0:T(8,128)S(1)}, f32[64,256]{1,0:T(8,128)S(1)}, u32[]{:S(2)}, u32[]{:S(2)}) collective-permute-start(f32[64,256]{1,0:T(8,128)S(1)} %get-tuple-element.55.refs_0_.refs_2_), channel_id=1, source_target_pairs={{0,1},{1,0},{2,3},{3,2},{4,5},{5,4},{6,7},{7,6},{8,9},{9,8},{10,11... | collective-permute-start | bytes 196616 | tf_op jit(solution)/shard_map/ppermute | solution.py:33
  60.2 10.6 %collective-permute-start.29 = (f32[64,256]{1,0:T(8,128)S(1)}, f32[64,256]{1,0:T(8,128)S(1)}, u32[]{:S(2)}, u32[]{:S(2)}) collective-permute-start(f32[64,256]{1,0:T(8,128)S(1)} %sub.21), channel_id=1, source_target_pairs={{0,3},{1,2},{2,1},{3,0},{4,7},{5,6},{6,5},{7,4},{8,11},{9,10},{10,... | collective-permute-start | bytes 196616 | tf_op jit(solution)/shard_map/ppermute | solution.py:33
  63.7 7.5 %collective-permute-start.28 = (f32[64,256]{1,0:T(8,128)S(1)}, f32[64,256]{1,0:T(8,128)S(1)}, u32[]{:S(2)}, u32[]{:S(2)}) collective-permute-start(f32[64,256]{1,0:T(8,128)S(1)} %sub.21), channel_id=1, source_target_pairs={{0,2},{1,3},{2,0},{3,1},{4,6},{5,7},{6,4},{7,5},{8,10},{9,11},{10,... | collective-permute-start | bytes 196616 | tf_op jit(solution)/shard_map/ppermute | solution.py:33
  63.9 5.6 %collective-permute-start.27 = (f32[64,256]{1,0:T(8,128)S(1)}, f32[64,256]{1,0:T(8,128)S(1)}, u32[]{:S(2)}, u32[]{:S(2)}) collective-permute-start(f32[64,256]{1,0:T(8,128)S(1)} %sub.21), channel_id=1, source_target_pairs={{0,1},{1,0},{2,3},{3,2},{4,5},{5,4},{6,7},{7,6},{8,9},{9,8},{10,11... | collective-permute-start | bytes 196616 | tf_op jit(solution)/shard_map/ppermute | solution.py:33
  65.9 10.6 %collective-permute-start.23 = (f32[64,256]{1,0:T(8,128)S(1)}, f32[64,256]{1,0:T(8,128)S(1)}, u32[]{:S(2)}, u32[]{:S(2)}) collective-permute-start(f32[64,256]{1,0:T(8,128)S(1)} %sub.20), channel_id=1, source_target_pairs={{0,3},{1,2},{2,1},{3,0},{4,7},{5,6},{6,5},{7,4},{8,11},{9,10},{10,... | collective-permute-start | bytes 196616 | tf_op jit(solution)/shard_map/ppermute | solution.py:33
  69.3 7.5 %collective-permute-start.22 = (f32[64,256]{1,0:T(8,128)S(1)}, f32[64,256]{1,0:T(8,128)S(1)}, u32[]{:S(2)}, u32[]{:S(2)}) collective-permute-start(f32[64,256]{1,0:T(8,128)S(1)} %sub.20), channel_id=1, source_target_pairs={{0,2},{1,3},{2,0},{3,1},{4,6},{5,7},{6,4},{7,5},{8,10},{9,11},{10,... | collective-permute-start | bytes 196616 | tf_op jit(solution)/shard_map/ppermute | solution.py:33
  69.5 5.7 %collective-permute-start.21 = (f32[64,256]{1,0:T(8,128)S(1)}, f32[64,256]{1,0:T(8,128)S(1)}, u32[]{:S(2)}, u32[]{:S(2)}) collective-permute-start(f32[64,256]{1,0:T(8,128)S(1)} %sub.20), channel_id=1, source_target_pairs={{0,1},{1,0},{2,3},{3,2},{4,5},{5,4},{6,7},{7,6},{8,9},{9,8},{10,11... | collective-permute-start | bytes 196616 | tf_op jit(solution)/shard_map/ppermute | solution.py:33
  71.8 10.9 %collective-permute-start.38 = (f32[64,256]{1,0:T(8,128)S(1)}, f32[64,256]{1,0:T(8,128)S(1)}, u32[]{:S(2)}, u32[]{:S(2)}) collective-permute-start(f32[64,256]{1,0:T(8,128)S(1)} %get-tuple-element.63.refs_5_), channel_id=1, source_target_pairs={{0,3},{1,2},{2,1},{3,0},{4,7},{5,6},{6,5},{7,4},{8,11},{9,10},{10,... | collective-permute-start | bytes 196616 | tf_op jit(solution)/shard_map/ppermute | solution.py:33
  75.2 7.8 %collective-permute-start.37 = (f32[64,256]{1,0:T(8,128)S(1)}, f32[64,256]{1,0:T(8,128)S(1)}, u32[]{:S(2)}, u32[]{:S(2)}) collective-permute-start(f32[64,256]{1,0:T(8,128)S(1)} %get-tuple-element.63.refs_5_), channel_id=1, source_target_pairs={{0,2},{1,3},{2,0},{3,1},{4,6},{5,7},{6,4},{7,5},{8,10},{9,11},{10,... | collective-permute-start | bytes 196616 | tf_op jit(solution)/shard_map/ppermute | solution.py:33
  75.2 6.1 %collective-permute-start.36 = (f32[64,256]{1,0:T(8,128)S(1)}, f32[64,256]{1,0:T(8,128)S(1)}, u32[]{:S(2)}, u32[]{:S(2)}) collective-permute-start(f32[64,256]{1,0:T(8,128)S(1)} %get-tuple-element.63.refs_5_), channel_id=1, source_target_pairs={{0,1},{1,0},{2,3},{3,2},{4,5},{5,4},{6,7},{7,6},{8,9},{9,8},{10,11... | collective-permute-start | bytes 196616 | tf_op jit(solution)/shard_map/ppermute | solution.py:33
  77.4 10.9 %collective-permute-start.32 = (f32[64,256]{1,0:T(8,128)S(1)}, f32[64,256]{1,0:T(8,128)S(1)}, u32[]{:S(2)}, u32[]{:S(2)}) collective-permute-start(f32[64,256]{1,0:T(8,128)S(1)} %get-tuple-element.57.refs_0_.refs_4_), channel_id=1, source_target_pairs={{0,3},{1,2},{2,1},{3,0},{4,7},{5,6},{6,5},{7,4},{8,11},{9,10},{10,... | collective-permute-start | bytes 196616 | tf_op jit(solution)/shard_map/ppermute | solution.py:33
  80.9 7.8 %collective-permute-start.31 = (f32[64,256]{1,0:T(8,128)S(1)}, f32[64,256]{1,0:T(8,128)S(1)}, u32[]{:S(2)}, u32[]{:S(2)}) collective-permute-start(f32[64,256]{1,0:T(8,128)S(1)} %get-tuple-element.57.refs_0_.refs_4_), channel_id=1, source_target_pairs={{0,2},{1,3},{2,0},{3,1},{4,6},{5,7},{6,4},{7,5},{8,10},{9,11},{10,... | collective-permute-start | bytes 196616 | tf_op jit(solution)/shard_map/ppermute | solution.py:33
  81.4 5.7 %collective-permute-start.30 = (f32[64,256]{1,0:T(8,128)S(1)}, f32[64,256]{1,0:T(8,128)S(1)}, u32[]{:S(2)}, u32[]{:S(2)}) collective-permute-start(f32[64,256]{1,0:T(8,128)S(1)} %get-tuple-element.57.refs_0_.refs_4_), channel_id=1, source_target_pairs={{0,1},{1,0},{2,3},{3,2},{4,5},{5,4},{6,7},{7,6},{8,9},{9,8},{10,11... | collective-permute-start | bytes 196616 | tf_op jit(solution)/shard_map/ppermute | solution.py:33
  83.6 21.3 %collective-permute-start.41 = (f32[64,256]{1,0:T(8,128)S(1)}, f32[64,256]{1,0:T(8,128)S(1)}, u32[]{:S(2)}, u32[]{:S(2)}) collective-permute-start(f32[64,256]{1,0:T(8,128)S(1)} %sub.23), channel_id=1, source_target_pairs={{0,3},{1,2},{2,1},{3,0},{4,7},{5,6},{6,5},{7,4},{8,11},{9,10},{10,... | collective-permute-start | bytes 196616 | tf_op jit(solution)/shard_map/ppermute | solution.py:33
  87.1 18.1 %collective-permute-start.40 = (f32[64,256]{1,0:T(8,128)S(1)}, f32[64,256]{1,0:T(8,128)S(1)}, u32[]{:S(2)}, u32[]{:S(2)}) collective-permute-start(f32[64,256]{1,0:T(8,128)S(1)} %sub.23), channel_id=1, source_target_pairs={{0,2},{1,3},{2,0},{3,1},{4,6},{5,7},{6,4},{7,5},{8,10},{9,11},{10,... | collective-permute-start | bytes 196616 | tf_op jit(solution)/shard_map/ppermute | solution.py:33
  87.1 17.5 %collective-permute-start.39 = (f32[64,256]{1,0:T(8,128)S(1)}, f32[64,256]{1,0:T(8,128)S(1)}, u32[]{:S(2)}, u32[]{:S(2)}) collective-permute-start(f32[64,256]{1,0:T(8,128)S(1)} %sub.23), channel_id=1, source_target_pairs={{0,1},{1,0},{2,3},{3,2},{4,5},{5,4},{6,7},{7,6},{8,9},{9,8},{10,11... | collective-permute-start | bytes 196616 | tf_op jit(solution)/shard_map/ppermute | solution.py:33
  88.4 29.0 %copy-start.5 = (f32[1,1,3,128,1024]{4,3,2,1,0:T(8,128)S(1)}, f32[1,1,3,128,1024]{4,3,2,1,0:T(8,128)}, u32[]{:S(2)}) copy-start(f32[1,1,3,128,1024]{4,3,2,1,0:T(8,128)} %param.13) | copy-start | bytes 4718596
  88.4 29.0 %copy-start.9 = (s32[1,1,3]{2,1,0:T(1,128)S(1)}, s32[1,1,3]{2,1,0:T(1,128)}, u32[]{:S(2)}) copy-start(s32[1,1,3]{2,1,0:T(1,128)} %refs_6_.1) | copy-start | bytes 40
  89.3 9.1 %collective-permute-start.35 = (f32[64,256]{1,0:T(8,128)S(1)}, f32[64,256]{1,0:T(8,128)S(1)}, u32[]{:S(2)}, u32[]{:S(2)}) collective-permute-start(f32[64,256]{1,0:T(8,128)S(1)} %sub.22), channel_id=1, source_target_pairs={{0,3},{1,2},{2,1},{3,0},{4,7},{5,6},{6,5},{7,4},{8,11},{9,10},{10,... | collective-permute-start | bytes 196616 | tf_op jit(solution)/shard_map/ppermute | solution.py:33
  92.7 5.3 %collective-permute-start.33 = (f32[64,256]{1,0:T(8,128)S(1)}, f32[64,256]{1,0:T(8,128)S(1)}, u32[]{:S(2)}, u32[]{:S(2)}) collective-permute-start(f32[64,256]{1,0:T(8,128)S(1)} %sub.22), channel_id=1, source_target_pairs={{0,1},{1,0},{2,3},{3,2},{4,5},{5,4},{6,7},{7,6},{8,9},{9,8},{10,11... | collective-permute-start | bytes 196616 | tf_op jit(solution)/shard_map/ppermute | solution.py:33
  98.1 5.9 %collective-permute-start.34 = (f32[64,256]{1,0:T(8,128)S(1)}, f32[64,256]{1,0:T(8,128)S(1)}, u32[]{:S(2)}, u32[]{:S(2)}) collective-permute-start(f32[64,256]{1,0:T(8,128)S(1)} %sub.22), channel_id=1, source_target_pairs={{0,2},{1,3},{2,0},{3,1},{4,6},{5,7},{6,4},{7,5},{8,10},{9,11},{10,... | collective-permute-start | bytes 196616 | tf_op jit(solution)/shard_map/ppermute | solution.py:33
  104.2 6.5 %collective-permute-start.42 = (f32[64,256]{1,0:T(8,128)S(1)}, f32[64,256]{1,0:T(8,128)S(1)}, u32[]{:S(2)}, u32[]{:S(2)}) collective-permute-start(f32[64,256]{1,0:T(8,128)S(1)} %get-tuple-element.59.refs_6_), channel_id=1, source_target_pairs={{0,1},{1,0},{2,3},{3,2},{4,5},{5,4},{6,7},{7,6},{8,9},{9,8},{10,11... | collective-permute-start | bytes 196616 | tf_op jit(solution)/shard_map/ppermute | solution.py:33
  105.5 13.1 %collective-permute-start.47 = (f32[64,256]{1,0:T(8,128)S(1)}, f32[64,256]{1,0:T(8,128)S(1)}, u32[]{:S(2)}, u32[]{:S(2)}) collective-permute-start(f32[64,256]{1,0:T(8,128)S(1)} %get-tuple-element.65.refs_7_), channel_id=1, source_target_pairs={{0,3},{1,2},{2,1},{3,0},{4,7},{5,6},{6,5},{7,4},{8,11},{9,10},{10,... | collective-permute-start | bytes 196616 | tf_op jit(solution)/shard_map/ppermute | solution.py:33
  106.3 12.3 %collective-permute-start.46 = (f32[64,256]{1,0:T(8,128)S(1)}, f32[64,256]{1,0:T(8,128)S(1)}, u32[]{:S(2)}, u32[]{:S(2)}) collective-permute-start(f32[64,256]{1,0:T(8,128)S(1)} %get-tuple-element.65.refs_7_), channel_id=1, source_target_pairs={{0,2},{1,3},{2,0},{3,1},{4,6},{5,7},{6,4},{7,5},{8,10},{9,11},{10,... | collective-permute-start | bytes 196616 | tf_op jit(solution)/shard_map/ppermute | solution.py:33
  108.8 9.8 %collective-permute-start.45 = (f32[64,256]{1,0:T(8,128)S(1)}, f32[64,256]{1,0:T(8,128)S(1)}, u32[]{:S(2)}, u32[]{:S(2)}) collective-permute-start(f32[64,256]{1,0:T(8,128)S(1)} %get-tuple-element.65.refs_7_), channel_id=1, source_target_pairs={{0,1},{1,0},{2,3},{3,2},{4,5},{5,4},{6,7},{7,6},{8,9},{9,8},{10,11... | collective-permute-start | bytes 196616 | tf_op jit(solution)/shard_map/ppermute | solution.py:33
  110.0 7.3 %collective-permute-start.44 = (f32[64,256]{1,0:T(8,128)S(1)}, f32[64,256]{1,0:T(8,128)S(1)}, u32[]{:S(2)}, u32[]{:S(2)}) collective-permute-start(f32[64,256]{1,0:T(8,128)S(1)} %get-tuple-element.59.refs_6_), channel_id=1, source_target_pairs={{0,3},{1,2},{2,1},{3,0},{4,7},{5,6},{6,5},{7,4},{8,11},{9,10},{10,... | collective-permute-start | bytes 196616 | tf_op jit(solution)/shard_map/ppermute | solution.py:33
  110.7 6.6 %collective-permute-start.43 = (f32[64,256]{1,0:T(8,128)S(1)}, f32[64,256]{1,0:T(8,128)S(1)}, u32[]{:S(2)}, u32[]{:S(2)}) collective-permute-start(f32[64,256]{1,0:T(8,128)S(1)} %get-tuple-element.59.refs_6_), channel_id=1, source_target_pairs={{0,2},{1,3},{2,0},{3,1},{4,6},{5,7},{6,4},{7,5},{8,10},{9,11},{10,... | collective-permute-start | bytes 196616 | tf_op jit(solution)/shard_map/ppermute | solution.py:33
  119.9 1.4 collective-permute-start.48
  121.3 4.6 %collective-permute-start.49 = (f32[2,16,512]{2,1,0:T(8,128)S(1)}, f32[2,16,512]{2,1,0:T(8,128)S(1)}, u32[]{:S(2)}, u32[]{:S(2)}) collective-permute-start(f32[2,16,512]{2,1,0:T(8,128)S(1)} %get-tuple-element.40), channel_id=1, source_target_pairs={{0,8},{4,12},{8,0},{12,4},{16,24},{20,28},{24,16},{28,20},{1,9},{5... | collective-permute-start | bytes 196616 | tf_op jit(solution)/shard_map/ppermute | solution.py:71
  122.9 4.3 %collective-permute-start.50 = (f32[2,16,512]{2,1,0:T(8,128)S(1)}, f32[2,16,512]{2,1,0:T(8,128)S(1)}, u32[]{:S(2)}, u32[]{:S(2)}) collective-permute-start(f32[2,16,512]{2,1,0:T(8,128)S(1)} %get-tuple-element.41), channel_id=1, source_target_pairs={{0,16},{4,20},{8,24},{12,28},{16,0},{20,4},{24,8},{28,12},{1,17},{... | collective-permute-start | bytes 196616 | tf_op jit(solution)/shard_map/ppermute | solution.py:71
  124.4 5.2 %collective-permute-start.51 = (f32[2,16,512]{2,1,0:T(8,128)S(1)}, f32[2,16,512]{2,1,0:T(8,128)S(1)}, u32[]{:S(2)}, u32[]{:S(2)}) collective-permute-start(f32[2,16,512]{2,1,0:T(8,128)S(1)} %get-tuple-element.42), channel_id=1, source_target_pairs={{0,24},{4,28},{8,16},{12,20},{16,8},{20,12},{24,0},{28,4},{1,25},{... | collective-permute-start | bytes 196616 | tf_op jit(solution)/shard_map/ppermute | solution.py:71
  130.0 4.9 %collective-permute-start.52 = (f32[16,1280]{1,0:T(8,128)S(1)}, f32[16,1280]{1,0:T(8,128)S(1)}, u32[]{:S(2)}, u32[]{:S(2)}) collective-permute-start(f32[16,1280]{1,0:T(8,128)S(1)} %get-tuple-element.45), channel_id=1, source_target_pairs={{0,1},{1,0},{2,3},{3,2},{4,5},{5,4},{6,7},{7,6},{8,9},{9,8},{10,11... | collective-permute-start | bytes 245768 | tf_op jit(solution)/shard_map/ppermute | solution.py:33
  130.2 7.2 %collective-permute-start.53 = (f32[16,1280]{1,0:T(8,128)S(1)}, f32[16,1280]{1,0:T(8,128)S(1)}, u32[]{:S(2)}, u32[]{:S(2)}) collective-permute-start(f32[16,1280]{1,0:T(8,128)S(1)} %get-tuple-element.46), channel_id=1, source_target_pairs={{0,2},{1,3},{2,0},{3,1},{4,6},{5,7},{6,4},{7,5},{8,10},{9,11},{10,... | collective-permute-start | bytes 245768 | tf_op jit(solution)/shard_map/ppermute | solution.py:33
  132.4 6.3 %collective-permute-start.54 = (f32[16,1280]{1,0:T(8,128)S(1)}, f32[16,1280]{1,0:T(8,128)S(1)}, u32[]{:S(2)}, u32[]{:S(2)}) collective-permute-start(f32[16,1280]{1,0:T(8,128)S(1)} %get-tuple-element.47), channel_id=1, source_target_pairs={{0,3},{1,2},{2,1},{3,0},{4,7},{5,6},{6,5},{7,4},{8,11},{9,10},{10,... | collective-permute-start | bytes 245768 | tf_op jit(solution)/shard_map/ppermute | solution.py:33
  139.1 5.6 %collective-permute-start.57 = (f32[16,256]{1,0:T(8,128)S(1)}, f32[16,256]{1,0:T(8,128)S(1)}, u32[]{:S(2)}, u32[]{:S(2)}) collective-permute-start(f32[16,256]{1,0:T(8,128)S(1)} %get-tuple-element.50.refs_0_.refs_6_), channel_id=1, source_target_pairs={{0,3},{1,2},{2,1},{3,0},{4,7},{5,6},{6,5},{7,4},{8,11},{9,10},{10,... | collective-permute-start | bytes 49160 | tf_op jit(solution)/shard_map/ppermute | solution.py:33
  141.2 4.6 %collective-permute-start.56 = (f32[16,256]{1,0:T(8,128)S(1)}, f32[16,256]{1,0:T(8,128)S(1)}, u32[]{:S(2)}, u32[]{:S(2)}) collective-permute-start(f32[16,256]{1,0:T(8,128)S(1)} %get-tuple-element.50.refs_0_.refs_6_), channel_id=1, source_target_pairs={{0,2},{1,3},{2,0},{3,1},{4,6},{5,7},{6,4},{7,5},{8,10},{9,11},{10,... | collective-permute-start | bytes 49160 | tf_op jit(solution)/shard_map/ppermute | solution.py:33
  141.7 4.1 %collective-permute-start.55 = (f32[16,256]{1,0:T(8,128)S(1)}, f32[16,256]{1,0:T(8,128)S(1)}, u32[]{:S(2)}, u32[]{:S(2)}) collective-permute-start(f32[16,256]{1,0:T(8,128)S(1)} %get-tuple-element.50.refs_0_.refs_6_), channel_id=1, source_target_pairs={{0,1},{1,0},{2,3},{3,2},{4,5},{5,4},{6,7},{7,6},{8,9},{9,8},{10,11... | collective-permute-start | bytes 49160 | tf_op jit(solution)/shard_map/ppermute | solution.py:33
  146.2 5.6 %collective-permute-start.60 = (f32[16,256]{1,0:T(8,128)S(1)}, f32[16,256]{1,0:T(8,128)S(1)}, u32[]{:S(2)}, u32[]{:S(2)}) collective-permute-start(f32[16,256]{1,0:T(8,128)S(1)} %shard_map.126.refs_0_), channel_id=1, source_target_pairs={{0,3},{1,2},{2,1},{3,0},{4,7},{5,6},{6,5},{7,4},{8,11},{9,10},{10,... | collective-permute-start | bytes 49160 | tf_op jit(solution)/shard_map/ppermute | solution.py:33
  148.0 4.6 %collective-permute-start.59 = (f32[16,256]{1,0:T(8,128)S(1)}, f32[16,256]{1,0:T(8,128)S(1)}, u32[]{:S(2)}, u32[]{:S(2)}) collective-permute-start(f32[16,256]{1,0:T(8,128)S(1)} %shard_map.126.refs_0_), channel_id=1, source_target_pairs={{0,2},{1,3},{2,0},{3,1},{4,6},{5,7},{6,4},{7,5},{8,10},{9,11},{10,... | collective-permute-start | bytes 49160 | tf_op jit(solution)/shard_map/ppermute | solution.py:33
  149.1 3.7 %collective-permute-start.58 = (f32[16,256]{1,0:T(8,128)S(1)}, f32[16,256]{1,0:T(8,128)S(1)}, u32[]{:S(2)}, u32[]{:S(2)}) collective-permute-start(f32[16,256]{1,0:T(8,128)S(1)} %shard_map.126.refs_0_), channel_id=1, source_target_pairs={{0,1},{1,0},{2,3},{3,2},{4,5},{5,4},{6,7},{7,6},{8,9},{9,8},{10,11... | collective-permute-start | bytes 49160 | tf_op jit(solution)/shard_map/ppermute | solution.py:33
  (8 other events, 83.8 us)

commit v14 on v13

--- a/solution.py
+++ b/solution.py
@@ -73,7 +73,6 @@
 
 VMEM = pl.BlockSpec(memory_space=pltpu.VMEM)
 SMEM = pl.BlockSpec(memory_space=pltpu.SMEM)
-HBM = pl.BlockSpec(memory_space=pltpu.HBM)
 ANY = pl.BlockSpec(memory_space=pl.ANY)
 
 
@@ -194,14 +193,38 @@
     )
 
 
-def turn(rhs, index, streams, after=None):
+def turn(rhs, first, last, streams):
     rows, count = rhs.shape[2:]
     depth = count // streams
-    extra = [] if after is None else [after]
+
+    def body(rhs_ref, out, held, sem):
+        copy = pltpu.make_async_copy(rhs_ref.at[0, first:last], held, sem)
+        copy.start()
+        copy.wait()
+        for index in range(last - first):
+            wide = jnp.transpose(held[index])
+            for i in range(streams):
+                out[index * streams + i] = wide[i * depth : (i + 1) * depth]
+
+    return local_kernel(
+        body,
+        [float_array(streams * (last - first), depth, rows)],
+        [rhs],
+        [ANY],
+        scratch=[
+            pltpu.VMEM((last - first, rows, count), jnp.float32),
+            pltpu.SemaphoreType.DMA(()),
+        ],
+    )[0]
+
+
+def turn_first(rhs, streams):
+    rows, count = rhs.shape[2:]
+    depth = count // streams
 
     def body(rhs_ref, *refs):
-        outs, (held, sem) = refs[len(extra) : -2], refs[-2:]
-        copy = pltpu.make_async_copy(rhs_ref.at[0, index], held, sem)
+        outs, (held, sem) = refs[:-2], refs[-2:]
+        copy = pltpu.make_async_copy(rhs_ref.at[0, 0], held, sem)
         copy.start()
         copy.wait()
         wide = jnp.transpose(held[...])
@@ -211,8 +234,8 @@
     return local_kernel(
         body,
         [float_array(depth, rows)] * streams,
-        [rhs, *extra],
-        [HBM] + [ANY] * len(extra),
+        [rhs],
+        [ANY],
         scratch=[pltpu.VMEM((rows, count), jnp.float32), pltpu.SemaphoreType.DMA(())],
     )
 
@@ -381,14 +404,14 @@
         body,
         [float_array(depth, rows)],
         [*held, factor],
-        [VMEM] * members + [HBM],
+        [VMEM] * members + [ANY],
         flops=6 * depth * rows * order,
         scratch=[
             pltpu.VMEM((depth, order), jnp.float32),
             pltpu.VMEM((rows, order), jnp.float32),
             pltpu.SemaphoreType.DMA(()),
         ],
-        limit=2**24,
+        limit=56 * 2**20,
     )[0]
 
 
@@ -441,7 +464,8 @@
     slots, tile_rows = tiles.shape[2:4]
 
     streams = 2 if rhs_count % 16 == 0 else 1
-    residuals = turn(rhs_local, 0, streams)
+    residuals = turn_first(rhs_local, streams)
+    later = turn(rhs_local, 1, supernodes, streams)
     solved = []
     gathered = []
     for current in range(supernodes):
@@ -456,9 +480,8 @@
         held = [gather_rows(value) for value in owned]
         gathered.append([assemble(pieces, order) for pieces in held])
         if current + 1 < supernodes:
-            turned = turn(rhs_local, current + 1, streams, owned[0])
             residuals = [
-                turned[i] - apply_pieces(sub_local, current, pieces)
+                later[current * streams + i] - apply_pieces(sub_local, current, pieces)
                 for i, pieces in enumerate(held)
             ]
 

time: 154 us -> 142 us (0.922)
  waiting for transfers between devices: 37.7 us -> 17.5 us
  Pallas kernels: 9.38 us -> 13.9 us
  starting transfers between devices: 86.8 us -> 90.1 us
    ppermute x57, waiting for transfers between devices: 32.6 us -> 12.4 us  [send(): return lax.ppermute(value, axis, pairs)]
    pallas_call x15 -> x13, Pallas kernels: 9.38 us -> 13.9 us  [local_kernel(): pl.pallas_call(body, out_shape=list(outs), in_specs=specs or [VMEM] * len...]
    ppermute x57, starting transfers between devices: 83.2 us -> 86.5 us  [send(): return lax.ppermute(value, axis, pairs)]
    unnamed x22 -> x24, local copies, waits for them, and re-layouts: 3.43 us -> 2.29 us
  transfers between devices with their start and end apart: 61 -> 61, of which waited for: 17 -> 12; matrix products, arithmetic and copies ran while one was open for 9% -> 11% of each run, Pallas kernels for 4% -> 7%
where the time goes in v14:
time: 142 us; the launch traced here: 141 us
  starting transfers between devices  90.1 us (63%)
  waiting for transfers between devices  17.5 us (12%)
  Pallas kernels  13.9 us (10%)
  matrix products  13.7 us (10%)
  local copies, waits for them, and re-layouts  3.59 us (3%)
  between operations  2.4 us (2%)
    ppermute x57, starting transfers between devices, send(): return lax.ppermute(value, axis, pairs)  86.5 us
    pallas_call x13, Pallas kernels, local_kernel(): pl.pallas_call(body, out_shape=list(outs), in_specs=specs or [VMEM] * len...  13.9 us
    dot_general x48, matrix products, contract_last(): lax.dot_general(left, right, (((left.ndim - 1,), (right.ndim - 1,)), ((),...  13.7 us
    ppermute x57, waiting for transfers between devices, send(): return lax.ppermute(value, axis, pairs)  12.4 us
    ppermute x3, waiting for transfers between devices, swap(): return lax.ppermute(value, axis, pairs)  3.7 us
    ppermute x3, starting transfers between devices, swap(): return lax.ppermute(value, axis, pairs)  3.55 us
  transfers between devices with their start and end apart: 61, of which 12 were waited for; matrix products, arithmetic and copies ran while one was open for 11% of the time, Pallas kernels for 7%

profile of v14, /device:TPU:0, one launch (start us, length us, event | category | flops | bytes accessed | tf_op | source)
XLA Modules:
  0.0 141.1 jit_solution(2993649138808950980)
XLA Ops:
  0.7 1.2 copy-done.2
  1.8 0.9 shard_map.113
  2.7 5.1 %collective-permute-start.2 = (f32[64,256]{1,0:T(8,128)}, f32[64,256]{1,0:T(8,128)}, u32[]{:S(2)}, u32[]{:S(2)}) collective-permute-start(f32[64,256]{1,0:T(8,128)} %get-tuple-element.22.refs_0_), channel_id=1, source_target_pairs={{0,3},{1,2},{2,1},{3,0},{4,7},{5,6},{6,5},{7,4},{8,11},{9,10},{10,... | collective-permute-start | bytes 196616 | tf_op jit(solution)/shard_map/ppermute | solution.py:33
  7.8 0.6 collective-permute-start
  8.5 3.7 %collective-permute-start.5 = (f32[64,256]{1,0:T(8,128)}, f32[64,256]{1,0:T(8,128)}, u32[]{:S(2)}, u32[]{:S(2)}) collective-permute-start(f32[64,256]{1,0:T(8,128)} %get-tuple-element.23.refs_0_), channel_id=1, source_target_pairs={{0,3},{1,2},{2,1},{3,0},{4,7},{5,6},{6,5},{7,4},{8,11},{9,10},{10,... | collective-permute-start | bytes 196616 | tf_op jit(solution)/shard_map/ppermute | solution.py:33
  12.2 1.1 collective-permute-start.3
  13.4 1.0 copy-done.3
  15.4 1.3 collective-permute-done.1.refs_2_
  16.7 3.2 %shard_map.114.refs_0_ = f32[64,256]{1,0:T(8,128)} custom-call(f32[64,256]{1,0:T(8,128)} %get-tuple-element.22.refs_0_, f32[64,256]{1,0:T(8,128)} %collective-permute-done.refs_1_, f32[64,256]{1,0:T(8,128)} %collective-permute-done.1.refs_2_, f32[64,256]{1,0:T(8,128)} %collective-permute-done.2.refs_3_, f32[1,4,256,1024]{3,2,1,0:T(8,128)} %refs_4_.3), custom_call_target="tpu_custom_call" | custom-call | flops 100663296 | bytes 4521984 | tf_op jit(solution)/shard_map/pallas_call | solution.py:81
  20.0 2.6 %collective-permute-start.8 = (f32[64,256]{1,0:T(8,128)}, f32[64,256]{1,0:T(8,128)S(1)}, u32[]{:S(2)}, u32[]{:S(2)}) collective-permute-start(f32[64,256]{1,0:T(8,128)} %shard_map.114.refs_0_), channel_id=1, source_target_pairs={{0,3},{1,2},{2,1},{3,0},{4,7},{5,6},{6,5},{7,4},{8,11},{9,10},{10,... | collective-permute-start | bytes 196616 | tf_op jit(solution)/shard_map/ppermute | solution.py:33
  22.7 1.8 %collective-permute-start.6 = (f32[64,256]{1,0:T(8,128)}, f32[64,256]{1,0:T(8,128)S(1)}, u32[]{:S(2)}, u32[]{:S(2)}) collective-permute-start(f32[64,256]{1,0:T(8,128)} %shard_map.114.refs_0_), channel_id=1, source_target_pairs={{0,1},{1,0},{2,3},{3,2},{4,5},{5,4},{6,7},{7,6},{8,9},{9,8},{10,11... | collective-permute-start | bytes 196616 | tf_op jit(solution)/shard_map/ppermute | solution.py:33
  24.5 3.2 %shard_map.115.refs_1_ = f32[64,256]{1,0:T(8,128)} custom-call(f32[64,256]{1,0:T(8,128)} %get-tuple-element.23.refs_0_, f32[64,256]{1,0:T(8,128)} %collective-permute-done.3.refs_1_, f32[64,256]{1,0:T(8,128)} %collective-permute-done.4.refs_2_, f32[64,256]{1,0:T(8,128)} %collective-permute-done.5.refs_3_, f32[1,4,256,1024]{3,2,1,0:T(8,128)} %refs_4_.3), custom_call_target="tpu_custom_call" | custom-call | flops 100663296 | bytes 4521984 | tf_op jit(solution)/shard_map/pallas_call | solution.py:81
  27.7 2.6 %collective-permute-start.14 = (f32[64,256]{1,0:T(8,128)}, f32[64,256]{1,0:T(8,128)S(1)}, u32[]{:S(2)}, u32[]{:S(2)}) collective-permute-start(f32[64,256]{1,0:T(8,128)} %shard_map.115.refs_1_), channel_id=1, source_target_pairs={{0,3},{1,2},{2,1},{3,0},{4,7},{5,6},{6,5},{7,4},{8,11},{9,10},{10,... | collective-permute-start | bytes 196616 | tf_op jit(solution)/shard_map/ppermute | solution.py:33
  30.5 0.9 constant_dynamic-update-slice_fusion.15
  31.3 1.9 %collective-permute-start.12 = (f32[64,256]{1,0:T(8,128)}, f32[64,256]{1,0:T(8,128)S(1)}, u32[]{:S(2)}, u32[]{:S(2)}) collective-permute-start(f32[64,256]{1,0:T(8,128)} %shard_map.115.refs_1_), channel_id=1, source_target_pairs={{0,1},{1,0},{2,3},{3,2},{4,5},{5,4},{6,7},{7,6},{8,9},{9,8},{10,11... | collective-permute-start | bytes 196616 | tf_op jit(solution)/shard_map/ppermute | solution.py:33
  34.7 2.6 %collective-permute-start.11 = (f32[64,256]{1,0:T(8,128)S(1)}, f32[64,256]{1,0:T(8,128)S(1)}, u32[]{:S(2)}, u32[]{:S(2)}) collective-permute-start(f32[64,256]{1,0:T(8,128)S(1)} %fusion.19), channel_id=1, source_target_pairs={{0,3},{1,2},{2,1},{3,0},{4,7},{5,6},{6,5},{7,4},{8,11},{9,10},{10,... | collective-permute-start | bytes 196616 | tf_op jit(solution)/shard_map/ppermute | solution.py:33
  37.3 1.8 %collective-permute-start.9 = (f32[64,256]{1,0:T(8,128)S(1)}, f32[64,256]{1,0:T(8,128)S(1)}, u32[]{:S(2)}, u32[]{:S(2)}) collective-permute-start(f32[64,256]{1,0:T(8,128)S(1)} %fusion.19), channel_id=1, source_target_pairs={{0,1},{1,0},{2,3},{3,2},{4,5},{5,4},{6,7},{7,6},{8,9},{9,8},{10,11... | collective-permute-start | bytes 196616 | tf_op jit(solution)/shard_map/ppermute | solution.py:33
  40.6 2.6 %collective-permute-start.17 = (f32[64,256]{1,0:T(8,128)S(1)}, f32[64,256]{1,0:T(8,128)S(1)}, u32[]{:S(2)}, u32[]{:S(2)}) collective-permute-start(f32[64,256]{1,0:T(8,128)S(1)} %fusion.15), channel_id=1, source_target_pairs={{0,3},{1,2},{2,1},{3,0},{4,7},{5,6},{6,5},{7,4},{8,11},{9,10},{10,... | collective-permute-start | bytes 196616 | tf_op jit(solution)/shard_map/ppermute | solution.py:33
  43.4 1.9 %collective-permute-start.15 = (f32[64,256]{1,0:T(8,128)S(1)}, f32[64,256]{1,0:T(8,128)S(1)}, u32[]{:S(2)}, u32[]{:S(2)}) collective-permute-start(f32[64,256]{1,0:T(8,128)S(1)} %fusion.15), channel_id=1, source_target_pairs={{0,1},{1,0},{2,3},{3,2},{4,5},{5,4},{6,7},{7,6},{8,9},{9,8},{10,11... | collective-permute-start | bytes 196616 | tf_op jit(solution)/shard_map/ppermute | solution.py:33
  46.5 2.6 %collective-permute-start.20 = (f32[64,256]{1,0:T(8,128)S(1)}, f32[64,256]{1,0:T(8,128)S(1)}, u32[]{:S(2)}, u32[]{:S(2)}) collective-permute-start(f32[64,256]{1,0:T(8,128)S(1)} %get-tuple-element.43.refs_2_), channel_id=1, source_target_pairs={{0,3},{1,2},{2,1},{3,0},{4,7},{5,6},{6,5},{7,4},{8,11},{9,10},{10,... | collective-permute-start | bytes 196616 | tf_op jit(solution)/shard_map/ppermute | solution.py:33
  49.1 1.8 %collective-permute-start.18 = (f32[64,256]{1,0:T(8,128)S(1)}, f32[64,256]{1,0:T(8,128)S(1)}, u32[]{:S(2)}, u32[]{:S(2)}) collective-permute-start(f32[64,256]{1,0:T(8,128)S(1)} %get-tuple-element.43.refs_2_), channel_id=1, source_target_pairs={{0,1},{1,0},{2,3},{3,2},{4,5},{5,4},{6,7},{7,6},{8,9},{9,8},{10,11... | collective-permute-start | bytes 196616 | tf_op jit(solution)/shard_map/ppermute | solution.py:33
  52.2 2.6 %collective-permute-start.26 = (f32[64,256]{1,0:T(8,128)S(1)}, f32[64,256]{1,0:T(8,128)S(1)}, u32[]{:S(2)}, u32[]{:S(2)}) collective-permute-start(f32[64,256]{1,0:T(8,128)S(1)} %get-tuple-element.49.refs_3_), channel_id=1, source_target_pairs={{0,3},{1,2},{2,1},{3,0},{4,7},{5,6},{6,5},{7,4},{8,11},{9,10},{10,... | collective-permute-start | bytes 196616 | tf_op jit(solution)/shard_map/ppermute | solution.py:33
  54.8 1.8 %collective-permute-start.24 = (f32[64,256]{1,0:T(8,128)S(1)}, f32[64,256]{1,0:T(8,128)S(1)}, u32[]{:S(2)}, u32[]{:S(2)}) collective-permute-start(f32[64,256]{1,0:T(8,128)S(1)} %get-tuple-element.49.refs_3_), channel_id=1, source_target_pairs={{0,1},{1,0},{2,3},{3,2},{4,5},{5,4},{6,7},{7,6},{8,9},{9,8},{10,11... | collective-permute-start | bytes 196616 | tf_op jit(solution)/shard_map/ppermute | solution.py:33
  57.8 2.6 %collective-permute-start.23 = (f32[64,256]{1,0:T(8,128)S(1)}, f32[64,256]{1,0:T(8,128)S(1)}, u32[]{:S(2)}, u32[]{:S(2)}) collective-permute-start(f32[64,256]{1,0:T(8,128)S(1)} %fusion.11), channel_id=1, source_target_pairs={{0,3},{1,2},{2,1},{3,0},{4,7},{5,6},{6,5},{7,4},{8,11},{9,10},{10,... | collective-permute-start | bytes 196616 | tf_op jit(solution)/shard_map/ppermute | solution.py:33
  60.5 1.8 %collective-permute-start.21 = (f32[64,256]{1,0:T(8,128)S(1)}, f32[64,256]{1,0:T(8,128)S(1)}, u32[]{:S(2)}, u32[]{:S(2)}) collective-permute-start(f32[64,256]{1,0:T(8,128)S(1)} %fusion.11), channel_id=1, source_target_pairs={{0,1},{1,0},{2,3},{3,2},{4,5},{5,4},{6,7},{7,6},{8,9},{9,8},{10,11... | collective-permute-start | bytes 196616 | tf_op jit(solution)/shard_map/ppermute | solution.py:33
  63.5 2.6 %collective-permute-start.29 = (f32[64,256]{1,0:T(8,128)S(1)}, f32[64,256]{1,0:T(8,128)S(1)}, u32[]{:S(2)}, u32[]{:S(2)}) collective-permute-start(f32[64,256]{1,0:T(8,128)S(1)} %fusion.8), channel_id=1, source_target_pairs={{0,3},{1,2},{2,1},{3,0},{4,7},{5,6},{6,5},{7,4},{8,11},{9,10},{10,... | collective-permute-start | bytes 196616 | tf_op jit(solution)/shard_map/ppermute | solution.py:33
  66.2 1.9 %collective-permute-start.27 = (f32[64,256]{1,0:T(8,128)S(1)}, f32[64,256]{1,0:T(8,128)S(1)}, u32[]{:S(2)}, u32[]{:S(2)}) collective-permute-start(f32[64,256]{1,0:T(8,128)S(1)} %fusion.8), channel_id=1, source_target_pairs={{0,1},{1,0},{2,3},{3,2},{4,5},{5,4},{6,7},{7,6},{8,9},{9,8},{10,11... | collective-permute-start | bytes 196616 | tf_op jit(solution)/shard_map/ppermute | solution.py:33
  69.3 2.6 %collective-permute-start.32 = (f32[64,256]{1,0:T(8,128)S(1)}, f32[64,256]{1,0:T(8,128)S(1)}, u32[]{:S(2)}, u32[]{:S(2)}) collective-permute-start(f32[64,256]{1,0:T(8,128)S(1)} %get-tuple-element.45.refs_4_), channel_id=1, source_target_pairs={{0,3},{1,2},{2,1},{3,0},{4,7},{5,6},{6,5},{7,4},{8,11},{9,10},{10,... | collective-permute-start | bytes 196616 | tf_op jit(solution)/shard_map/ppermute | solution.py:33
  72.0 1.8 %collective-permute-start.30 = (f32[64,256]{1,0:T(8,128)S(1)}, f32[64,256]{1,0:T(8,128)S(1)}, u32[]{:S(2)}, u32[]{:S(2)}) collective-permute-start(f32[64,256]{1,0:T(8,128)S(1)} %get-tuple-element.45.refs_4_), channel_id=1, source_target_pairs={{0,1},{1,0},{2,3},{3,2},{4,5},{5,4},{6,7},{7,6},{8,9},{9,8},{10,11... | collective-permute-start | bytes 196616 | tf_op jit(solution)/shard_map/ppermute | solution.py:33
  75.0 2.6 %collective-permute-start.38 = (f32[64,256]{1,0:T(8,128)S(1)}, f32[64,256]{1,0:T(8,128)S(1)}, u32[]{:S(2)}, u32[]{:S(2)}) collective-permute-start(f32[64,256]{1,0:T(8,128)S(1)} %get-tuple-element.51.refs_5_), channel_id=1, source_target_pairs={{0,3},{1,2},{2,1},{3,0},{4,7},{5,6},{6,5},{7,4},{8,11},{9,10},{10,... | collective-permute-start | bytes 196616 | tf_op jit(solution)/shard_map/ppermute | solution.py:33
  77.6 1.8 %collective-permute-start.36 = (f32[64,256]{1,0:T(8,128)S(1)}, f32[64,256]{1,0:T(8,128)S(1)}, u32[]{:S(2)}, u32[]{:S(2)}) collective-permute-start(f32[64,256]{1,0:T(8,128)S(1)} %get-tuple-element.51.refs_5_), channel_id=1, source_target_pairs={{0,1},{1,0},{2,3},{3,2},{4,5},{5,4},{6,7},{7,6},{8,9},{9,8},{10,11... | collective-permute-start | bytes 196616 | tf_op jit(solution)/shard_map/ppermute | solution.py:33
  80.7 2.6 %collective-permute-start.35 = (f32[64,256]{1,0:T(8,128)S(1)}, f32[64,256]{1,0:T(8,128)S(1)}, u32[]{:S(2)}, u32[]{:S(2)}) collective-permute-start(f32[64,256]{1,0:T(8,128)S(1)} %fusion.5), channel_id=1, source_target_pairs={{0,3},{1,2},{2,1},{3,0},{4,7},{5,6},{6,5},{7,4},{8,11},{9,10},{10,... | collective-permute-start | bytes 196616 | tf_op jit(solution)/shard_map/ppermute | solution.py:33
  83.3 1.8 %collective-permute-start.33 = (f32[64,256]{1,0:T(8,128)S(1)}, f32[64,256]{1,0:T(8,128)S(1)}, u32[]{:S(2)}, u32[]{:S(2)}) collective-permute-start(f32[64,256]{1,0:T(8,128)S(1)} %fusion.5), channel_id=1, source_target_pairs={{0,1},{1,0},{2,3},{3,2},{4,5},{5,4},{6,7},{7,6},{8,9},{9,8},{10,11... | collective-permute-start | bytes 196616 | tf_op jit(solution)/shard_map/ppermute | solution.py:33
  86.3 2.6 %collective-permute-start.41 = (f32[64,256]{1,0:T(8,128)S(1)}, f32[64,256]{1,0:T(8,128)S(1)}, u32[]{:S(2)}, u32[]{:S(2)}) collective-permute-start(f32[64,256]{1,0:T(8,128)S(1)} %fusion.2), channel_id=1, source_target_pairs={{0,3},{1,2},{2,1},{3,0},{4,7},{5,6},{6,5},{7,4},{8,11},{9,10},{10,... | collective-permute-start | bytes 196616 | tf_op jit(solution)/shard_map/ppermute | solution.py:33
  89.1 1.9 %collective-permute-start.39 = (f32[64,256]{1,0:T(8,128)S(1)}, f32[64,256]{1,0:T(8,128)S(1)}, u32[]{:S(2)}, u32[]{:S(2)}) collective-permute-start(f32[64,256]{1,0:T(8,128)S(1)} %fusion.2), channel_id=1, source_target_pairs={{0,1},{1,0},{2,3},{3,2},{4,5},{5,4},{6,7},{7,6},{8,9},{9,8},{10,11... | collective-permute-start | bytes 196616 | tf_op jit(solution)/shard_map/ppermute | solution.py:33
  91.9 2.6 %collective-permute-start.44 = (f32[64,256]{1,0:T(8,128)S(1)}, f32[64,256]{1,0:T(8,128)S(1)}, u32[]{:S(2)}, u32[]{:S(2)}) collective-permute-start(f32[64,256]{1,0:T(8,128)S(1)} %get-tuple-element.47.refs_6_), channel_id=1, source_target_pairs={{0,3},{1,2},{2,1},{3,0},{4,7},{5,6},{6,5},{7,4},{8,11},{9,10},{10,... | collective-permute-start | bytes 196616 | tf_op jit(solution)/shard_map/ppermute | solution.py:33
  94.5 1.8 %collective-permute-start.42 = (f32[64,256]{1,0:T(8,128)S(1)}, f32[64,256]{1,0:T(8,128)S(1)}, u32[]{:S(2)}, u32[]{:S(2)}) collective-permute-start(f32[64,256]{1,0:T(8,128)S(1)} %get-tuple-element.47.refs_6_), channel_id=1, source_target_pairs={{0,1},{1,0},{2,3},{3,2},{4,5},{5,4},{6,7},{7,6},{8,9},{9,8},{10,11... | collective-permute-start | bytes 196616 | tf_op jit(solution)/shard_map/ppermute | solution.py:33
  97.3 2.6 %collective-permute-start.47 = (f32[64,256]{1,0:T(8,128)S(1)}, f32[64,256]{1,0:T(8,128)S(1)}, u32[]{:S(2)}, u32[]{:S(2)}) collective-permute-start(f32[64,256]{1,0:T(8,128)S(1)} %get-tuple-element.53.refs_7_), channel_id=1, source_target_pairs={{0,3},{1,2},{2,1},{3,0},{4,7},{5,6},{6,5},{7,4},{8,11},{9,10},{10,... | collective-permute-start | bytes 196616 | tf_op jit(solution)/shard_map/ppermute | solution.py:33
  99.9 1.8 %collective-permute-start.45 = (f32[64,256]{1,0:T(8,128)S(1)}, f32[64,256]{1,0:T(8,128)S(1)}, u32[]{:S(2)}, u32[]{:S(2)}) collective-permute-start(f32[64,256]{1,0:T(8,128)S(1)} %get-tuple-element.53.refs_7_), channel_id=1, source_target_pairs={{0,1},{1,0},{2,3},{3,2},{4,5},{5,4},{6,7},{7,6},{8,9},{9,8},{10,11... | collective-permute-start | bytes 196616 | tf_op jit(solution)/shard_map/ppermute | solution.py:33
  101.9 1.2 shard_map.117.refs_0_
  103.1 1.1 collective-permute-done.45
  104.2 0.9 collective-permute-done.46
  105.1 1.4 %shard_map.118 = (f32[4,16,512]{2,1,0:T(8,128)S(1)}, f32[4,16,512]{2,1,0:T(8,128)S(1)}) custom-call(f32[64,384]{1,0:T(8,128)S(1)} %shard_map.117.refs_0_, f32[64,1024]{1,0:T(8,128)S(1)} %constant_dynamic-update-slice_fusion.12.refs_1_, f32[64,1024]{1,0:T(8,128)S(1)} %constant_dynamic-update-slice_fusion.8.refs_2_, ...), custom_call_target="tpu_custom_call" | custom-call | flops 150994944 | bytes 2981916 | tf_op jit(solution)/shard_map/pallas_call | solution.py:81
  106.6 1.3 collective-permute-done.48.refs_1_
  107.9 1.6 %collective-permute-start.49 = (f32[2,16,512]{2,1,0:T(8,128)S(1)}, f32[2,16,512]{2,1,0:T(8,128)S(1)}, u32[]{:S(2)}, u32[]{:S(2)}) collective-permute-start(f32[2,16,512]{2,1,0:T(8,128)S(1)} %get-tuple-element.28), channel_id=1, source_target_pairs={{0,8},{4,12},{8,0},{12,4},{16,24},{20,28},{24,16},{28,20},{1,9},{5... | collective-permute-start | bytes 196616 | tf_op jit(solution)/shard_map/ppermute | solution.py:71
  109.5 1.5 %collective-permute-start.50 = (f32[2,16,512]{2,1,0:T(8,128)S(1)}, f32[2,16,512]{2,1,0:T(8,128)S(1)}, u32[]{:S(2)}, u32[]{:S(2)}) collective-permute-start(f32[2,16,512]{2,1,0:T(8,128)S(1)} %get-tuple-element.29), channel_id=1, source_target_pairs={{0,16},{4,20},{8,24},{12,28},{16,0},{20,4},{24,8},{28,12},{1,17},{... | collective-permute-start | bytes 196616 | tf_op jit(solution)/shard_map/ppermute | solution.py:71
  111.5 1.0 shard_map.119
  112.5 1.3 collective-permute-done.50.refs_2_
  113.8 2.4 %collective-permute-done.51.refs_3_ = f32[2,16,512]{2,1,0:T(8,128)S(1)} collective-permute-done((f32[2,16,512]{2,1,0:T(8,128)S(1)}, f32[2,16,512]{2,1,0:T(8,128)S(1)}, u32[]{:S(2)}, u32[]{:S(2)}) %collective-permute-start.51) | collective-permute-done | bytes 65568 | tf_op jit(solution)/shard_map/ppermute | solution.py:71
  116.6 1.2 collective-permute-start.52
  117.8 1.7 %collective-permute-start.53 = (f32[16,1280]{1,0:T(8,128)S(1)}, f32[16,1280]{1,0:T(8,128)S(1)}, u32[]{:S(2)}, u32[]{:S(2)}) collective-permute-start(f32[16,1280]{1,0:T(8,128)S(1)} %get-tuple-element.34), channel_id=1, source_target_pairs={{0,2},{1,3},{2,0},{3,1},{4,6},{5,7},{6,4},{7,5},{8,10},{9,11},{10,... | collective-permute-start | bytes 245768 | tf_op jit(solution)/shard_map/ppermute | solution.py:33
  119.5 1.5 %collective-permute-start.54 = (f32[16,1280]{1,0:T(8,128)S(1)}, f32[16,1280]{1,0:T(8,128)S(1)}, u32[]{:S(2)}, u32[]{:S(2)}) collective-permute-start(f32[16,1280]{1,0:T(8,128)S(1)} %get-tuple-element.35), channel_id=1, source_target_pairs={{0,3},{1,2},{2,1},{3,0},{4,7},{5,6},{6,5},{7,4},{8,11},{9,10},{10,... | collective-permute-start | bytes 245768 | tf_op jit(solution)/shard_map/ppermute | solution.py:33
  121.5 3.2 %collective-permute-done.53.refs_2_ = f32[16,1280]{1,0:T(8,128)S(1)} collective-permute-done((f32[16,1280]{1,0:T(8,128)S(1)}, f32[16,1280]{1,0:T(8,128)S(1)}, u32[]{:S(2)}, u32[]{:S(2)}) %collective-permute-start.53) | collective-permute-done | bytes 81952 | tf_op jit(solution)/shard_map/ppermute | solution.py:33
  124.7 1.1 collective-permute-done.54.refs_3_
  126.2 2.2 %collective-permute-start.57 = (f32[16,256]{1,0:T(8,128)S(1)}, f32[16,256]{1,0:T(8,128)S(1)}, u32[]{:S(2)}, u32[]{:S(2)}) collective-permute-start(f32[16,256]{1,0:T(8,128)S(1)} %get-tuple-element.38.refs_0_.refs_6_), channel_id=1, source_target_pairs={{0,3},{1,2},{2,1},{3,0},{4,7},{5,6},{6,5},{7,4},{8,11},{9,10},{10,... | collective-permute-start | bytes 49160 | tf_op jit(solution)/shard_map/ppermute | solution.py:33
  128.9 1.7 %collective-permute-start.55 = (f32[16,256]{1,0:T(8,128)S(1)}, f32[16,256]{1,0:T(8,128)S(1)}, u32[]{:S(2)}, u32[]{:S(2)}) collective-permute-start(f32[16,256]{1,0:T(8,128)S(1)} %get-tuple-element.38.refs_0_.refs_6_), channel_id=1, source_target_pairs={{0,1},{1,0},{2,3},{3,2},{4,5},{5,4},{6,7},{7,6},{8,9},{9,8},{10,11... | collective-permute-start | bytes 49160 | tf_op jit(solution)/shard_map/ppermute | solution.py:33
  130.6 1.1 collective-permute-done.57.refs_3_
  131.8 1.5 %collective-permute-done.56.refs_2_ = f32[16,256]{1,0:T(8,128)S(1)} collective-permute-done((f32[16,256]{1,0:T(8,128)S(1)}, f32[16,256]{1,0:T(8,128)S(1)}, u32[]{:S(2)}, u32[]{:S(2)}) %collective-permute-start.56) | collective-permute-done | bytes 16416 | tf_op jit(solution)/shard_map/ppermute | solution.py:33
  133.7 1.8 %collective-permute-start.60 = (f32[16,256]{1,0:T(8,128)S(1)}, f32[16,256]{1,0:T(8,128)S(1)}, u32[]{:S(2)}, u32[]{:S(2)}) collective-permute-start(f32[16,256]{1,0:T(8,128)S(1)} %shard_map.124.refs_0_), channel_id=1, source_target_pairs={{0,3},{1,2},{2,1},{3,0},{4,7},{5,6},{6,5},{7,4},{8,11},{9,10},{10,... | collective-permute-start | bytes 49160 | tf_op jit(solution)/shard_map/ppermute | solution.py:33
  135.4 0.8 collective-permute-start.59
  136.2 1.9 %collective-permute-start.58 = (f32[16,256]{1,0:T(8,128)S(1)}, f32[16,256]{1,0:T(8,128)S(1)}, u32[]{:S(2)}, u32[]{:S(2)}) collective-permute-start(f32[16,256]{1,0:T(8,128)S(1)} %shard_map.124.refs_0_), channel_id=1, source_target_pairs={{0,1},{1,0},{2,3},{3,2},{4,5},{5,4},{6,7},{7,6},{8,9},{9,8},{10,11... | collective-permute-start | bytes 49160 | tf_op jit(solution)/shard_map/ppermute | solution.py:33
  138.1 1.1 collective-permute-done.60.refs_3_
  139.2 0.9 collective-permute-done.59.refs_2_
  140.1 1.0 shard_map.125
  (177 shorter events, 17.3 us)
Async XLA Ops:
  0.6 32.6 %copy-start = (f32[1,3,256,1024]{3,2,1,0:T(8,128)S(1)}, f32[1,3,256,1024]{3,2,1,0:T(8,128)}, u32[]{:S(2)}) copy-start(f32[1,3,256,1024]{3,2,1,0:T(8,128)} %param.12) | copy-start | bytes 9437188
  2.7 9.5 %collective-permute-start.2 = (f32[64,256]{1,0:T(8,128)}, f32[64,256]{1,0:T(8,128)}, u32[]{:S(2)}, u32[]{:S(2)}) collective-permute-start(f32[64,256]{1,0:T(8,128)} %get-tuple-element.22.refs_0_), channel_id=1, source_target_pairs={{0,3},{1,2},{2,1},{3,0},{4,7},{5,6},{6,5},{7,4},{8,11},{9,10},{10,... | collective-permute-start | bytes 196616 | tf_op jit(solution)/shard_map/ppermute | solution.py:33
  7.8 8.9 %collective-permute-start.1 = (f32[64,256]{1,0:T(8,128)}, f32[64,256]{1,0:T(8,128)}, u32[]{:S(2)}, u32[]{:S(2)}) collective-permute-start(f32[64,256]{1,0:T(8,128)} %get-tuple-element.22.refs_0_), channel_id=1, source_target_pairs={{0,2},{1,3},{2,0},{3,1},{4,6},{5,7},{6,4},{7,5},{8,10},{9,11},{10,... | collective-permute-start | bytes 196616 | tf_op jit(solution)/shard_map/ppermute | solution.py:33
  7.8 8.9 %collective-permute-start = (f32[64,256]{1,0:T(8,128)}, f32[64,256]{1,0:T(8,128)}, u32[]{:S(2)}, u32[]{:S(2)}) collective-permute-start(f32[64,256]{1,0:T(8,128)} %get-tuple-element.22.refs_0_), channel_id=1, source_target_pairs={{0,1},{1,0},{2,3},{3,2},{4,5},{5,4},{6,7},{7,6},{8,9},{9,8},{10,11... | collective-permute-start | bytes 196616 | tf_op jit(solution)/shard_map/ppermute | solution.py:33
  8.5 14.2 %collective-permute-start.5 = (f32[64,256]{1,0:T(8,128)}, f32[64,256]{1,0:T(8,128)}, u32[]{:S(2)}, u32[]{:S(2)}) collective-permute-start(f32[64,256]{1,0:T(8,128)} %get-tuple-element.23.refs_0_), channel_id=1, source_target_pairs={{0,3},{1,2},{2,1},{3,0},{4,7},{5,6},{6,5},{7,4},{8,11},{9,10},{10,... | collective-permute-start | bytes 196616 | tf_op jit(solution)/shard_map/ppermute | solution.py:33
  12.2 12.3 %collective-permute-start.4 = (f32[64,256]{1,0:T(8,128)}, f32[64,256]{1,0:T(8,128)}, u32[]{:S(2)}, u32[]{:S(2)}) collective-permute-start(f32[64,256]{1,0:T(8,128)} %get-tuple-element.23.refs_0_), channel_id=1, source_target_pairs={{0,2},{1,3},{2,0},{3,1},{4,6},{5,7},{6,4},{7,5},{8,10},{9,11},{10,... | collective-permute-start | bytes 196616 | tf_op jit(solution)/shard_map/ppermute | solution.py:33
  12.2 12.2 %collective-permute-start.3 = (f32[64,256]{1,0:T(8,128)}, f32[64,256]{1,0:T(8,128)}, u32[]{:S(2)}, u32[]{:S(2)}) collective-permute-start(f32[64,256]{1,0:T(8,128)} %get-tuple-element.23.refs_0_), channel_id=1, source_target_pairs={{0,1},{1,0},{2,3},{3,2},{4,5},{5,4},{6,7},{7,6},{8,9},{9,8},{10,11... | collective-permute-start | bytes 196616 | tf_op jit(solution)/shard_map/ppermute | solution.py:33
  20.0 11.3 %collective-permute-start.8 = (f32[64,256]{1,0:T(8,128)}, f32[64,256]{1,0:T(8,128)S(1)}, u32[]{:S(2)}, u32[]{:S(2)}) collective-permute-start(f32[64,256]{1,0:T(8,128)} %shard_map.114.refs_0_), channel_id=1, source_target_pairs={{0,3},{1,2},{2,1},{3,0},{4,7},{5,6},{6,5},{7,4},{8,11},{9,10},{10,... | collective-permute-start | bytes 196616 | tf_op jit(solution)/shard_map/ppermute | solution.py:33
  22.7 10.8 %collective-permute-start.7 = (f32[64,256]{1,0:T(8,128)}, f32[64,256]{1,0:T(8,128)S(1)}, u32[]{:S(2)}, u32[]{:S(2)}) collective-permute-start(f32[64,256]{1,0:T(8,128)} %shard_map.114.refs_0_), channel_id=1, source_target_pairs={{0,2},{1,3},{2,0},{3,1},{4,6},{5,7},{6,4},{7,5},{8,10},{9,11},{10,... | collective-permute-start | bytes 196616 | tf_op jit(solution)/shard_map/ppermute | solution.py:33
  22.7 11.1 %collective-permute-start.6 = (f32[64,256]{1,0:T(8,128)}, f32[64,256]{1,0:T(8,128)S(1)}, u32[]{:S(2)}, u32[]{:S(2)}) collective-permute-start(f32[64,256]{1,0:T(8,128)} %shard_map.114.refs_0_), channel_id=1, source_target_pairs={{0,1},{1,0},{2,3},{3,2},{4,5},{5,4},{6,7},{7,6},{8,9},{9,8},{10,11... | collective-permute-start | bytes 196616 | tf_op jit(solution)/shard_map/ppermute | solution.py:33
  27.7 9.6 %collective-permute-start.14 = (f32[64,256]{1,0:T(8,128)}, f32[64,256]{1,0:T(8,128)S(1)}, u32[]{:S(2)}, u32[]{:S(2)}) collective-permute-start(f32[64,256]{1,0:T(8,128)} %shard_map.115.refs_1_), channel_id=1, source_target_pairs={{0,3},{1,2},{2,1},{3,0},{4,7},{5,6},{6,5},{7,4},{8,11},{9,10},{10,... | collective-permute-start | bytes 196616 | tf_op jit(solution)/shard_map/ppermute | solution.py:33
  30.4 9.0 %collective-permute-start.13 = (f32[64,256]{1,0:T(8,128)}, f32[64,256]{1,0:T(8,128)S(1)}, u32[]{:S(2)}, u32[]{:S(2)}) collective-permute-start(f32[64,256]{1,0:T(8,128)} %shard_map.115.refs_1_), channel_id=1, source_target_pairs={{0,2},{1,3},{2,0},{3,1},{4,6},{5,7},{6,4},{7,5},{8,10},{9,11},{10,... | collective-permute-start | bytes 196616 | tf_op jit(solution)/shard_map/ppermute | solution.py:33
  31.3 8.4 %collective-permute-start.12 = (f32[64,256]{1,0:T(8,128)}, f32[64,256]{1,0:T(8,128)S(1)}, u32[]{:S(2)}, u32[]{:S(2)}) collective-permute-start(f32[64,256]{1,0:T(8,128)} %shard_map.115.refs_1_), channel_id=1, source_target_pairs={{0,1},{1,0},{2,3},{3,2},{4,5},{5,4},{6,7},{7,6},{8,9},{9,8},{10,11... | collective-permute-start | bytes 196616 | tf_op jit(solution)/shard_map/ppermute | solution.py:33
  34.7 10.9 %collective-permute-start.11 = (f32[64,256]{1,0:T(8,128)S(1)}, f32[64,256]{1,0:T(8,128)S(1)}, u32[]{:S(2)}, u32[]{:S(2)}) collective-permute-start(f32[64,256]{1,0:T(8,128)S(1)} %fusion.19), channel_id=1, source_target_pairs={{0,3},{1,2},{2,1},{3,0},{4,7},{5,6},{6,5},{7,4},{8,11},{9,10},{10,... | collective-permute-start | bytes 196616 | tf_op jit(solution)/shard_map/ppermute | solution.py:33
  37.3 8.6 %collective-permute-start.10 = (f32[64,256]{1,0:T(8,128)S(1)}, f32[64,256]{1,0:T(8,128)S(1)}, u32[]{:S(2)}, u32[]{:S(2)}) collective-permute-start(f32[64,256]{1,0:T(8,128)S(1)} %fusion.19), channel_id=1, source_target_pairs={{0,2},{1,3},{2,0},{3,1},{4,6},{5,7},{6,4},{7,5},{8,10},{9,11},{10,... | collective-permute-start | bytes 196616 | tf_op jit(solution)/shard_map/ppermute | solution.py:33
  37.3 6.1 %collective-permute-start.9 = (f32[64,256]{1,0:T(8,128)S(1)}, f32[64,256]{1,0:T(8,128)S(1)}, u32[]{:S(2)}, u32[]{:S(2)}) collective-permute-start(f32[64,256]{1,0:T(8,128)S(1)} %fusion.19), channel_id=1, source_target_pairs={{0,1},{1,0},{2,3},{3,2},{4,5},{5,4},{6,7},{7,6},{8,9},{9,8},{10,11... | collective-permute-start | bytes 196616 | tf_op jit(solution)/shard_map/ppermute | solution.py:33
  40.6 10.6 %collective-permute-start.17 = (f32[64,256]{1,0:T(8,128)S(1)}, f32[64,256]{1,0:T(8,128)S(1)}, u32[]{:S(2)}, u32[]{:S(2)}) collective-permute-start(f32[64,256]{1,0:T(8,128)S(1)} %fusion.15), channel_id=1, source_target_pairs={{0,3},{1,2},{2,1},{3,0},{4,7},{5,6},{6,5},{7,4},{8,11},{9,10},{10,... | collective-permute-start | bytes 196616 | tf_op jit(solution)/shard_map/ppermute | solution.py:33
  43.3 8.3 %collective-permute-start.16 = (f32[64,256]{1,0:T(8,128)S(1)}, f32[64,256]{1,0:T(8,128)S(1)}, u32[]{:S(2)}, u32[]{:S(2)}) collective-permute-start(f32[64,256]{1,0:T(8,128)S(1)} %fusion.15), channel_id=1, source_target_pairs={{0,2},{1,3},{2,0},{3,1},{4,6},{5,7},{6,4},{7,5},{8,10},{9,11},{10,... | collective-permute-start | bytes 196616 | tf_op jit(solution)/shard_map/ppermute | solution.py:33
  43.4 5.7 %collective-permute-start.15 = (f32[64,256]{1,0:T(8,128)S(1)}, f32[64,256]{1,0:T(8,128)S(1)}, u32[]{:S(2)}, u32[]{:S(2)}) collective-permute-start(f32[64,256]{1,0:T(8,128)S(1)} %fusion.15), channel_id=1, source_target_pairs={{0,1},{1,0},{2,3},{3,2},{4,5},{5,4},{6,7},{7,6},{8,9},{9,8},{10,11... | collective-permute-start | bytes 196616 | tf_op jit(solution)/shard_map/ppermute | solution.py:33
  46.5 10.4 %collective-permute-start.20 = (f32[64,256]{1,0:T(8,128)S(1)}, f32[64,256]{1,0:T(8,128)S(1)}, u32[]{:S(2)}, u32[]{:S(2)}) collective-permute-start(f32[64,256]{1,0:T(8,128)S(1)} %get-tuple-element.43.refs_2_), channel_id=1, source_target_pairs={{0,3},{1,2},{2,1},{3,0},{4,7},{5,6},{6,5},{7,4},{8,11},{9,10},{10,... | collective-permute-start | bytes 196616 | tf_op jit(solution)/shard_map/ppermute | solution.py:33
  49.1 8.1 %collective-permute-start.19 = (f32[64,256]{1,0:T(8,128)S(1)}, f32[64,256]{1,0:T(8,128)S(1)}, u32[]{:S(2)}, u32[]{:S(2)}) collective-permute-start(f32[64,256]{1,0:T(8,128)S(1)} %get-tuple-element.43.refs_2_), channel_id=1, source_target_pairs={{0,2},{1,3},{2,0},{3,1},{4,6},{5,7},{6,4},{7,5},{8,10},{9,11},{10,... | collective-permute-start | bytes 196616 | tf_op jit(solution)/shard_map/ppermute | solution.py:33
  49.1 5.7 %collective-permute-start.18 = (f32[64,256]{1,0:T(8,128)S(1)}, f32[64,256]{1,0:T(8,128)S(1)}, u32[]{:S(2)}, u32[]{:S(2)}) collective-permute-start(f32[64,256]{1,0:T(8,128)S(1)} %get-tuple-element.43.refs_2_), channel_id=1, source_target_pairs={{0,1},{1,0},{2,3},{3,2},{4,5},{5,4},{6,7},{7,6},{8,9},{9,8},{10,11... | collective-permute-start | bytes 196616 | tf_op jit(solution)/shard_map/ppermute | solution.py:33
  52.2 10.4 %collective-permute-start.26 = (f32[64,256]{1,0:T(8,128)S(1)}, f32[64,256]{1,0:T(8,128)S(1)}, u32[]{:S(2)}, u32[]{:S(2)}) collective-permute-start(f32[64,256]{1,0:T(8,128)S(1)} %get-tuple-element.49.refs_3_), channel_id=1, source_target_pairs={{0,3},{1,2},{2,1},{3,0},{4,7},{5,6},{6,5},{7,4},{8,11},{9,10},{10,... | collective-permute-start | bytes 196616 | tf_op jit(solution)/shard_map/ppermute | solution.py:33
  54.8 8.1 %collective-permute-start.25 = (f32[64,256]{1,0:T(8,128)S(1)}, f32[64,256]{1,0:T(8,128)S(1)}, u32[]{:S(2)}, u32[]{:S(2)}) collective-permute-start(f32[64,256]{1,0:T(8,128)S(1)} %get-tuple-element.49.refs_3_), channel_id=1, source_target_pairs={{0,2},{1,3},{2,0},{3,1},{4,6},{5,7},{6,4},{7,5},{8,10},{9,11},{10,... | collective-permute-start | bytes 196616 | tf_op jit(solution)/shard_map/ppermute | solution.py:33
  54.8 5.6 %collective-permute-start.24 = (f32[64,256]{1,0:T(8,128)S(1)}, f32[64,256]{1,0:T(8,128)S(1)}, u32[]{:S(2)}, u32[]{:S(2)}) collective-permute-start(f32[64,256]{1,0:T(8,128)S(1)} %get-tuple-element.49.refs_3_), channel_id=1, source_target_pairs={{0,1},{1,0},{2,3},{3,2},{4,5},{5,4},{6,7},{7,6},{8,9},{9,8},{10,11... | collective-permute-start | bytes 196616 | tf_op jit(solution)/shard_map/ppermute | solution.py:33
  57.8 10.6 %collective-permute-start.23 = (f32[64,256]{1,0:T(8,128)S(1)}, f32[64,256]{1,0:T(8,128)S(1)}, u32[]{:S(2)}, u32[]{:S(2)}) collective-permute-start(f32[64,256]{1,0:T(8,128)S(1)} %fusion.11), channel_id=1, source_target_pairs={{0,3},{1,2},{2,1},{3,0},{4,7},{5,6},{6,5},{7,4},{8,11},{9,10},{10,... | collective-permute-start | bytes 196616 | tf_op jit(solution)/shard_map/ppermute | solution.py:33
  60.5 8.3 %collective-permute-start.22 = (f32[64,256]{1,0:T(8,128)S(1)}, f32[64,256]{1,0:T(8,128)S(1)}, u32[]{:S(2)}, u32[]{:S(2)}) collective-permute-start(f32[64,256]{1,0:T(8,128)S(1)} %fusion.11), channel_id=1, source_target_pairs={{0,2},{1,3},{2,0},{3,1},{4,6},{5,7},{6,4},{7,5},{8,10},{9,11},{10,... | collective-permute-start | bytes 196616 | tf_op jit(solution)/shard_map/ppermute | solution.py:33
  60.5 5.8 %collective-permute-start.21 = (f32[64,256]{1,0:T(8,128)S(1)}, f32[64,256]{1,0:T(8,128)S(1)}, u32[]{:S(2)}, u32[]{:S(2)}) collective-permute-start(f32[64,256]{1,0:T(8,128)S(1)} %fusion.11), channel_id=1, source_target_pairs={{0,1},{1,0},{2,3},{3,2},{4,5},{5,4},{6,7},{7,6},{8,9},{9,8},{10,11... | collective-permute-start | bytes 196616 | tf_op jit(solution)/shard_map/ppermute | solution.py:33
  63.5 10.6 %collective-permute-start.29 = (f32[64,256]{1,0:T(8,128)S(1)}, f32[64,256]{1,0:T(8,128)S(1)}, u32[]{:S(2)}, u32[]{:S(2)}) collective-permute-start(f32[64,256]{1,0:T(8,128)S(1)} %fusion.8), channel_id=1, source_target_pairs={{0,3},{1,2},{2,1},{3,0},{4,7},{5,6},{6,5},{7,4},{8,11},{9,10},{10,... | collective-permute-start | bytes 196616 | tf_op jit(solution)/shard_map/ppermute | solution.py:33
  66.1 8.3 %collective-permute-start.28 = (f32[64,256]{1,0:T(8,128)S(1)}, f32[64,256]{1,0:T(8,128)S(1)}, u32[]{:S(2)}, u32[]{:S(2)}) collective-permute-start(f32[64,256]{1,0:T(8,128)S(1)} %fusion.8), channel_id=1, source_target_pairs={{0,2},{1,3},{2,0},{3,1},{4,6},{5,7},{6,4},{7,5},{8,10},{9,11},{10,... | collective-permute-start | bytes 196616 | tf_op jit(solution)/shard_map/ppermute | solution.py:33
  66.2 5.7 %collective-permute-start.27 = (f32[64,256]{1,0:T(8,128)S(1)}, f32[64,256]{1,0:T(8,128)S(1)}, u32[]{:S(2)}, u32[]{:S(2)}) collective-permute-start(f32[64,256]{1,0:T(8,128)S(1)} %fusion.8), channel_id=1, source_target_pairs={{0,1},{1,0},{2,3},{3,2},{4,5},{5,4},{6,7},{7,6},{8,9},{9,8},{10,11... | collective-permute-start | bytes 196616 | tf_op jit(solution)/shard_map/ppermute | solution.py:33
  69.3 10.4 %collective-permute-start.32 = (f32[64,256]{1,0:T(8,128)S(1)}, f32[64,256]{1,0:T(8,128)S(1)}, u32[]{:S(2)}, u32[]{:S(2)}) collective-permute-start(f32[64,256]{1,0:T(8,128)S(1)} %get-tuple-element.45.refs_4_), channel_id=1, source_target_pairs={{0,3},{1,2},{2,1},{3,0},{4,7},{5,6},{6,5},{7,4},{8,11},{9,10},{10,... | collective-permute-start | bytes 196616 | tf_op jit(solution)/shard_map/ppermute | solution.py:33
  72.0 8.1 %collective-permute-start.31 = (f32[64,256]{1,0:T(8,128)S(1)}, f32[64,256]{1,0:T(8,128)S(1)}, u32[]{:S(2)}, u32[]{:S(2)}) collective-permute-start(f32[64,256]{1,0:T(8,128)S(1)} %get-tuple-element.45.refs_4_), channel_id=1, source_target_pairs={{0,2},{1,3},{2,0},{3,1},{4,6},{5,7},{6,4},{7,5},{8,10},{9,11},{10,... | collective-permute-start | bytes 196616 | tf_op jit(solution)/shard_map/ppermute | solution.py:33
  72.0 5.7 %collective-permute-start.30 = (f32[64,256]{1,0:T(8,128)S(1)}, f32[64,256]{1,0:T(8,128)S(1)}, u32[]{:S(2)}, u32[]{:S(2)}) collective-permute-start(f32[64,256]{1,0:T(8,128)S(1)} %get-tuple-element.45.refs_4_), channel_id=1, source_target_pairs={{0,1},{1,0},{2,3},{3,2},{4,5},{5,4},{6,7},{7,6},{8,9},{9,8},{10,11... | collective-permute-start | bytes 196616 | tf_op jit(solution)/shard_map/ppermute | solution.py:33
  75.0 10.4 %collective-permute-start.38 = (f32[64,256]{1,0:T(8,128)S(1)}, f32[64,256]{1,0:T(8,128)S(1)}, u32[]{:S(2)}, u32[]{:S(2)}) collective-permute-start(f32[64,256]{1,0:T(8,128)S(1)} %get-tuple-element.51.refs_5_), channel_id=1, source_target_pairs={{0,3},{1,2},{2,1},{3,0},{4,7},{5,6},{6,5},{7,4},{8,11},{9,10},{10,... | collective-permute-start | bytes 196616 | tf_op jit(solution)/shard_map/ppermute | solution.py:33
  77.6 8.1 %collective-permute-start.37 = (f32[64,256]{1,0:T(8,128)S(1)}, f32[64,256]{1,0:T(8,128)S(1)}, u32[]{:S(2)}, u32[]{:S(2)}) collective-permute-start(f32[64,256]{1,0:T(8,128)S(1)} %get-tuple-element.51.refs_5_), channel_id=1, source_target_pairs={{0,2},{1,3},{2,0},{3,1},{4,6},{5,7},{6,4},{7,5},{8,10},{9,11},{10,... | collective-permute-start | bytes 196616 | tf_op jit(solution)/shard_map/ppermute | solution.py:33
  77.6 5.7 %collective-permute-start.36 = (f32[64,256]{1,0:T(8,128)S(1)}, f32[64,256]{1,0:T(8,128)S(1)}, u32[]{:S(2)}, u32[]{:S(2)}) collective-permute-start(f32[64,256]{1,0:T(8,128)S(1)} %get-tuple-element.51.refs_5_), channel_id=1, source_target_pairs={{0,1},{1,0},{2,3},{3,2},{4,5},{5,4},{6,7},{7,6},{8,9},{9,8},{10,11... | collective-permute-start | bytes 196616 | tf_op jit(solution)/shard_map/ppermute | solution.py:33
  80.7 21.2 %copy-start.1 = (f32[1,1,3,128,1024]{4,3,2,1,0:T(8,128)S(1)}, f32[1,1,3,128,1024]{4,3,2,1,0:T(8,128)}, u32[]{:S(2)}) copy-start(f32[1,1,3,128,1024]{4,3,2,1,0:T(8,128)} %param.13) | copy-start | bytes 4718596
  80.7 21.2 %copy-start.9 = (s32[1,1,3]{2,1,0:T(1,128)S(1)}, s32[1,1,3]{2,1,0:T(1,128)}, u32[]{:S(2)}) copy-start(s32[1,1,3]{2,1,0:T(1,128)} %refs_6_.1) | copy-start | bytes 40
  80.7 10.6 %collective-permute-start.35 = (f32[64,256]{1,0:T(8,128)S(1)}, f32[64,256]{1,0:T(8,128)S(1)}, u32[]{:S(2)}, u32[]{:S(2)}) collective-permute-start(f32[64,256]{1,0:T(8,128)S(1)} %fusion.5), channel_id=1, source_target_pairs={{0,3},{1,2},{2,1},{3,0},{4,7},{5,6},{6,5},{7,4},{8,11},{9,10},{10,... | collective-permute-start | bytes 196616 | tf_op jit(solution)/shard_map/ppermute | solution.py:33
  83.3 8.3 %collective-permute-start.34 = (f32[64,256]{1,0:T(8,128)S(1)}, f32[64,256]{1,0:T(8,128)S(1)}, u32[]{:S(2)}, u32[]{:S(2)}) collective-permute-start(f32[64,256]{1,0:T(8,128)S(1)} %fusion.5), channel_id=1, source_target_pairs={{0,2},{1,3},{2,0},{3,1},{4,6},{5,7},{6,4},{7,5},{8,10},{9,11},{10,... | collective-permute-start | bytes 196616 | tf_op jit(solution)/shard_map/ppermute | solution.py:33
  83.3 5.8 %collective-permute-start.33 = (f32[64,256]{1,0:T(8,128)S(1)}, f32[64,256]{1,0:T(8,128)S(1)}, u32[]{:S(2)}, u32[]{:S(2)}) collective-permute-start(f32[64,256]{1,0:T(8,128)S(1)} %fusion.5), channel_id=1, source_target_pairs={{0,1},{1,0},{2,3},{3,2},{4,5},{5,4},{6,7},{7,6},{8,9},{9,8},{10,11... | collective-permute-start | bytes 196616 | tf_op jit(solution)/shard_map/ppermute | solution.py:33
  86.3 10.3 %collective-permute-start.41 = (f32[64,256]{1,0:T(8,128)S(1)}, f32[64,256]{1,0:T(8,128)S(1)}, u32[]{:S(2)}, u32[]{:S(2)}) collective-permute-start(f32[64,256]{1,0:T(8,128)S(1)} %fusion.2), channel_id=1, source_target_pairs={{0,3},{1,2},{2,1},{3,0},{4,7},{5,6},{6,5},{7,4},{8,11},{9,10},{10,... | collective-permute-start | bytes 196616 | tf_op jit(solution)/shard_map/ppermute | solution.py:33
  89.0 8.0 %collective-permute-start.40 = (f32[64,256]{1,0:T(8,128)S(1)}, f32[64,256]{1,0:T(8,128)S(1)}, u32[]{:S(2)}, u32[]{:S(2)}) collective-permute-start(f32[64,256]{1,0:T(8,128)S(1)} %fusion.2), channel_id=1, source_target_pairs={{0,2},{1,3},{2,0},{3,1},{4,6},{5,7},{6,4},{7,5},{8,10},{9,11},{10,... | collective-permute-start | bytes 196616 | tf_op jit(solution)/shard_map/ppermute | solution.py:33
  89.1 5.5 %collective-permute-start.39 = (f32[64,256]{1,0:T(8,128)S(1)}, f32[64,256]{1,0:T(8,128)S(1)}, u32[]{:S(2)}, u32[]{:S(2)}) collective-permute-start(f32[64,256]{1,0:T(8,128)S(1)} %fusion.2), channel_id=1, source_target_pairs={{0,1},{1,0},{2,3},{3,2},{4,5},{5,4},{6,7},{7,6},{8,9},{9,8},{10,11... | collective-permute-start | bytes 196616 | tf_op jit(solution)/shard_map/ppermute | solution.py:33
  91.9 9.9 %collective-permute-start.44 = (f32[64,256]{1,0:T(8,128)S(1)}, f32[64,256]{1,0:T(8,128)S(1)}, u32[]{:S(2)}, u32[]{:S(2)}) collective-permute-start(f32[64,256]{1,0:T(8,128)S(1)} %get-tuple-element.47.refs_6_), channel_id=1, source_target_pairs={{0,3},{1,2},{2,1},{3,0},{4,7},{5,6},{6,5},{7,4},{8,11},{9,10},{10,... | collective-permute-start | bytes 196616 | tf_op jit(solution)/shard_map/ppermute | solution.py:33
  94.5 7.2 %collective-permute-start.43 = (f32[64,256]{1,0:T(8,128)S(1)}, f32[64,256]{1,0:T(8,128)S(1)}, u32[]{:S(2)}, u32[]{:S(2)}) collective-permute-start(f32[64,256]{1,0:T(8,128)S(1)} %get-tuple-element.47.refs_6_), channel_id=1, source_target_pairs={{0,2},{1,3},{2,0},{3,1},{4,6},{5,7},{6,4},{7,5},{8,10},{9,11},{10,... | collective-permute-start | bytes 196616 | tf_op jit(solution)/shard_map/ppermute | solution.py:33
  94.5 5.4 %collective-permute-start.42 = (f32[64,256]{1,0:T(8,128)S(1)}, f32[64,256]{1,0:T(8,128)S(1)}, u32[]{:S(2)}, u32[]{:S(2)}) collective-permute-start(f32[64,256]{1,0:T(8,128)S(1)} %get-tuple-element.47.refs_6_), channel_id=1, source_target_pairs={{0,1},{1,0},{2,3},{3,2},{4,5},{5,4},{6,7},{7,6},{8,9},{9,8},{10,11... | collective-permute-start | bytes 196616 | tf_op jit(solution)/shard_map/ppermute | solution.py:33
  97.3 7.8 %collective-permute-start.47 = (f32[64,256]{1,0:T(8,128)S(1)}, f32[64,256]{1,0:T(8,128)S(1)}, u32[]{:S(2)}, u32[]{:S(2)}) collective-permute-start(f32[64,256]{1,0:T(8,128)S(1)} %get-tuple-element.53.refs_7_), channel_id=1, source_target_pairs={{0,3},{1,2},{2,1},{3,0},{4,7},{5,6},{6,5},{7,4},{8,11},{9,10},{10,... | collective-permute-start | bytes 196616 | tf_op jit(solution)/shard_map/ppermute | solution.py:33
  99.9 5.2 %collective-permute-start.46 = (f32[64,256]{1,0:T(8,128)S(1)}, f32[64,256]{1,0:T(8,128)S(1)}, u32[]{:S(2)}, u32[]{:S(2)}) collective-permute-start(f32[64,256]{1,0:T(8,128)S(1)} %get-tuple-element.53.refs_7_), channel_id=1, source_target_pairs={{0,2},{1,3},{2,0},{3,1},{4,6},{5,7},{6,4},{7,5},{8,10},{9,11},{10,... | collective-permute-start | bytes 196616 | tf_op jit(solution)/shard_map/ppermute | solution.py:33
  99.9 4.3 %collective-permute-start.45 = (f32[64,256]{1,0:T(8,128)S(1)}, f32[64,256]{1,0:T(8,128)S(1)}, u32[]{:S(2)}, u32[]{:S(2)}) collective-permute-start(f32[64,256]{1,0:T(8,128)S(1)} %get-tuple-element.53.refs_7_), channel_id=1, source_target_pairs={{0,1},{1,0},{2,3},{3,2},{4,5},{5,4},{6,7},{7,6},{8,9},{9,8},{10,11... | collective-permute-start | bytes 196616 | tf_op jit(solution)/shard_map/ppermute | solution.py:33
  106.6 1.4 collective-permute-start.48
  107.9 4.6 %collective-permute-start.49 = (f32[2,16,512]{2,1,0:T(8,128)S(1)}, f32[2,16,512]{2,1,0:T(8,128)S(1)}, u32[]{:S(2)}, u32[]{:S(2)}) collective-permute-start(f32[2,16,512]{2,1,0:T(8,128)S(1)} %get-tuple-element.28), channel_id=1, source_target_pairs={{0,8},{4,12},{8,0},{12,4},{16,24},{20,28},{24,16},{28,20},{1,9},{5... | collective-permute-start | bytes 196616 | tf_op jit(solution)/shard_map/ppermute | solution.py:71
  109.5 4.3 %collective-permute-start.50 = (f32[2,16,512]{2,1,0:T(8,128)S(1)}, f32[2,16,512]{2,1,0:T(8,128)S(1)}, u32[]{:S(2)}, u32[]{:S(2)}) collective-permute-start(f32[2,16,512]{2,1,0:T(8,128)S(1)} %get-tuple-element.29), channel_id=1, source_target_pairs={{0,16},{4,20},{8,24},{12,28},{16,0},{20,4},{24,8},{28,12},{1,17},{... | collective-permute-start | bytes 196616 | tf_op jit(solution)/shard_map/ppermute | solution.py:71
  111.0 5.2 %collective-permute-start.51 = (f32[2,16,512]{2,1,0:T(8,128)S(1)}, f32[2,16,512]{2,1,0:T(8,128)S(1)}, u32[]{:S(2)}, u32[]{:S(2)}) collective-permute-start(f32[2,16,512]{2,1,0:T(8,128)S(1)} %get-tuple-element.30), channel_id=1, source_target_pairs={{0,24},{4,28},{8,16},{12,20},{16,8},{20,12},{24,0},{28,4},{1,25},{... | collective-permute-start | bytes 196616 | tf_op jit(solution)/shard_map/ppermute | solution.py:71
  116.6 4.9 %collective-permute-start.52 = (f32[16,1280]{1,0:T(8,128)S(1)}, f32[16,1280]{1,0:T(8,128)S(1)}, u32[]{:S(2)}, u32[]{:S(2)}) collective-permute-start(f32[16,1280]{1,0:T(8,128)S(1)} %get-tuple-element.33), channel_id=1, source_target_pairs={{0,1},{1,0},{2,3},{3,2},{4,5},{5,4},{6,7},{7,6},{8,9},{9,8},{10,11... | collective-permute-start | bytes 245768 | tf_op jit(solution)/shard_map/ppermute | solution.py:33
  117.8 6.9 %collective-permute-start.53 = (f32[16,1280]{1,0:T(8,128)S(1)}, f32[16,1280]{1,0:T(8,128)S(1)}, u32[]{:S(2)}, u32[]{:S(2)}) collective-permute-start(f32[16,1280]{1,0:T(8,128)S(1)} %get-tuple-element.34), channel_id=1, source_target_pairs={{0,2},{1,3},{2,0},{3,1},{4,6},{5,7},{6,4},{7,5},{8,10},{9,11},{10,... | collective-permute-start | bytes 245768 | tf_op jit(solution)/shard_map/ppermute | solution.py:33
  119.5 6.3 %collective-permute-start.54 = (f32[16,1280]{1,0:T(8,128)S(1)}, f32[16,1280]{1,0:T(8,128)S(1)}, u32[]{:S(2)}, u32[]{:S(2)}) collective-permute-start(f32[16,1280]{1,0:T(8,128)S(1)} %get-tuple-element.35), channel_id=1, source_target_pairs={{0,3},{1,2},{2,1},{3,0},{4,7},{5,6},{6,5},{7,4},{8,11},{9,10},{10,... | collective-permute-start | bytes 245768 | tf_op jit(solution)/shard_map/ppermute | solution.py:33
  126.2 5.6 %collective-permute-start.57 = (f32[16,256]{1,0:T(8,128)S(1)}, f32[16,256]{1,0:T(8,128)S(1)}, u32[]{:S(2)}, u32[]{:S(2)}) collective-permute-start(f32[16,256]{1,0:T(8,128)S(1)} %get-tuple-element.38.refs_0_.refs_6_), channel_id=1, source_target_pairs={{0,3},{1,2},{2,1},{3,0},{4,7},{5,6},{6,5},{7,4},{8,11},{9,10},{10,... | collective-permute-start | bytes 49160 | tf_op jit(solution)/shard_map/ppermute | solution.py:33
  128.4 4.9 %collective-permute-start.56 = (f32[16,256]{1,0:T(8,128)S(1)}, f32[16,256]{1,0:T(8,128)S(1)}, u32[]{:S(2)}, u32[]{:S(2)}) collective-permute-start(f32[16,256]{1,0:T(8,128)S(1)} %get-tuple-element.38.refs_0_.refs_6_), channel_id=1, source_target_pairs={{0,2},{1,3},{2,0},{3,1},{4,6},{5,7},{6,4},{7,5},{8,10},{9,11},{10,... | collective-permute-start | bytes 49160 | tf_op jit(solution)/shard_map/ppermute | solution.py:33
  128.9 4.4 %collective-permute-start.55 = (f32[16,256]{1,0:T(8,128)S(1)}, f32[16,256]{1,0:T(8,128)S(1)}, u32[]{:S(2)}, u32[]{:S(2)}) collective-permute-start(f32[16,256]{1,0:T(8,128)S(1)} %get-tuple-element.38.refs_0_.refs_6_), channel_id=1, source_target_pairs={{0,1},{1,0},{2,3},{3,2},{4,5},{5,4},{6,7},{7,6},{8,9},{9,8},{10,11... | collective-permute-start | bytes 49160 | tf_op jit(solution)/shard_map/ppermute | solution.py:33
  133.7 5.6 %collective-permute-start.60 = (f32[16,256]{1,0:T(8,128)S(1)}, f32[16,256]{1,0:T(8,128)S(1)}, u32[]{:S(2)}, u32[]{:S(2)}) collective-permute-start(f32[16,256]{1,0:T(8,128)S(1)} %shard_map.124.refs_0_), channel_id=1, source_target_pairs={{0,3},{1,2},{2,1},{3,0},{4,7},{5,6},{6,5},{7,4},{8,11},{9,10},{10,... | collective-permute-start | bytes 49160 | tf_op jit(solution)/shard_map/ppermute | solution.py:33
  135.4 4.7 %collective-permute-start.59 = (f32[16,256]{1,0:T(8,128)S(1)}, f32[16,256]{1,0:T(8,128)S(1)}, u32[]{:S(2)}, u32[]{:S(2)}) collective-permute-start(f32[16,256]{1,0:T(8,128)S(1)} %shard_map.124.refs_0_), channel_id=1, source_target_pairs={{0,2},{1,3},{2,0},{3,1},{4,6},{5,7},{6,4},{7,5},{8,10},{9,11},{10,... | collective-permute-start | bytes 49160 | tf_op jit(solution)/shard_map/ppermute | solution.py:33
  136.2 3.9 %collective-permute-start.58 = (f32[16,256]{1,0:T(8,128)S(1)}, f32[16,256]{1,0:T(8,128)S(1)}, u32[]{:S(2)}, u32[]{:S(2)}) collective-permute-start(f32[16,256]{1,0:T(8,128)S(1)} %shard_map.124.refs_0_), channel_id=1, source_target_pairs={{0,1},{1,0},{2,3},{3,2},{4,5},{5,4},{6,7},{7,6},{8,9},{9,8},{10,11... | collective-permute-start | bytes 49160 | tf_op jit(solution)/shard_map/ppermute | solution.py:33
  (9 other events, 105.9 us)

commit v15 on v14

--- a/solution.py
+++ b/solution.py
@@ -49,6 +49,22 @@
     for offset, piece in pieces:
         whole = lax.dynamic_update_slice_in_dim(whole, piece, offset, 1)
     return whole
+
+
+def pair_up(pieces):
+    members = len(pieces)
+    if members & (members - 1) or members == 1:
+        return pieces
+    pairs = []
+    for at in range(0, members, 2):
+        (first, left), (second, right) = pieces[at : at + 2]
+        rows, width = left.shape
+        both = jnp.zeros((rows, 2 * width), jnp.float32)
+        begin = jnp.minimum(first, second)
+        both = lax.dynamic_update_slice_in_dim(both, left, first - begin, 1)
+        both = lax.dynamic_update_slice_in_dim(both, right, second - begin, 1)
+        pairs.append((begin, both))
+    return pairs
 
 
 def apply_pieces(factor, index, pieces):
@@ -385,36 +401,6 @@
         whole[:, j * width : (j + 1) * width] = value
 
 
-def apply_first(value, factor):
-    members = lax.axis_size("grp")
-    depth, width = value.shape
-    rows, order = factor.shape[2:]
-    held = [value] + [send(value, "grp", distance) for distance in range(1, members)]
-
-    def body(*refs):
-        factor_ref, out, whole, matrix, sem = refs[members:]
-        copy = pltpu.make_async_copy(factor_ref.at[0, 0], matrix, sem)
-        copy.start()
-        put_in_order([refs[d][...] for d in range(members)], whole)
-        copy.wait()
-        top, rest = high_low(matrix[...])
-        out[...] = split_product(whole[...], top, rest)
-
-    return local_kernel(
-        body,
-        [float_array(depth, rows)],
-        [*held, factor],
-        [VMEM] * members + [ANY],
-        flops=6 * depth * rows * order,
-        scratch=[
-            pltpu.VMEM((depth, order), jnp.float32),
-            pltpu.VMEM((rows, order), jnp.float32),
-            pltpu.SemaphoreType.DMA(()),
-        ],
-        limit=56 * 2**20,
-    )[0]
-
-
 def apply_split(pieces, top, rest, index, base=None, begin=0, others=None):
     members = lax.axis_size("grp")
     part, width = pieces[0].shape
@@ -443,6 +429,25 @@
         flops=6 * part * rows * order,
         scratch=[pltpu.VMEM((part, order), jnp.float32)],
     )[0]
+
+
+def split_first(factor):
+    rows, order = factor.shape[2:]
+
+    def body(factor_ref, top, rest, matrix, sem):
+        copy = pltpu.make_async_copy(factor_ref.at[0, 0], matrix, sem)
+        copy.start()
+        copy.wait()
+        top[0], rest[0] = high_low(matrix[...])
+
+    return local_kernel(
+        body,
+        [jax.ShapeDtypeStruct((1, rows, order), jnp.bfloat16)] * 2,
+        [factor],
+        [ANY],
+        scratch=[pltpu.VMEM((rows, order), jnp.float32), pltpu.SemaphoreType.DMA(())],
+        limit=56 * 2**20,
+    )
 
 
 def on_device(
@@ -466,18 +471,20 @@
     streams = 2 if rhs_count % 16 == 0 else 1
     residuals = turn_first(rhs_local, streams)
     later = turn(rhs_local, 1, supernodes, streams)
+    first_top, first_rest = split_first(diag_inv_local)
     solved = []
     gathered = []
     for current in range(supernodes):
         owned = []
         for residual in residuals:
+            pieces = gather_rows(residual)
             if current:
-                pieces = gather_rows(residual)
-                owned.append(apply_pieces(diag_inv_local, current, pieces))
+                owned.append(apply_pieces(diag_inv_local, current, pair_up(pieces)))
             else:
-                owned.append(apply_first(residual, diag_inv_local))
+                values = [piece for _, piece in pieces]
+                owned.append(apply_split(values, first_top, first_rest, 0))
         solved.append(owned)
-        held = [gather_rows(value) for value in owned]
+        held = [pair_up(gather_rows(value)) for value in owned]
         gathered.append([assemble(pieces, order) for pieces in held])
         if current + 1 < supernodes:
             residuals = [

time: 142 us -> 321 us (2.26); the launches traced: 141 us -> 317 us
  local copies, waits for them, and re-layouts: 3.59 us -> 147 us
  matrix products: 13.7 us -> 48.6 us
    dynamic_update_slice x0 -> x56, local copies, waits for them, and re-layouts: none -> 83.8 us  [the longest x28 42.2 us: pair_up(): both = lax.dynamic_update_slice_in_dim(both, left, first - begin, 1)]
    dot_general x48 -> x24, matrix products: 13.7 us -> 48.6 us  [contract_last(): lax.dot_general(left, right, (((left.ndim - 1,), (right.ndim - 1,)), ((),...]
    dynamic_update_slice x26 -> x16, local copies, waits for them, and re-layouts: 1.15 us -> 26.7 us  [assemble(): whole = lax.dynamic_update_slice_in_dim(whole, piece, offset, 1)]
    another operation x8 -> x36, local copies, waits for them, and re-layouts: 0.15 us -> 21 us
    unnamed x24 -> x46, local copies, waits for them, and re-layouts: 2.29 us -> 15.3 us
    pallas_call x13 -> x14, Pallas kernels: 13.9 us -> 13.6 us  [local_kernel(): pl.pallas_call(body, out_shape=list(outs), in_specs=specs or [VMEM] * len...]
  transfers between devices with their start and end apart: 61 -> 61, of which waited for: 12 -> 9; matrix products, arithmetic and copies ran while one was open for 11% -> 56% of each run, Pallas kernels for 7% -> 3%
where the time goes in v15:
time: 321 us; the launch traced here: 317 us
  local copies, waits for them, and re-layouts  147 us (46%)
  starting transfers between devices  90.2 us (28%)
  matrix products  48.6 us (15%)
  waiting for transfers between devices  15.9 us (5%)
  Pallas kernels  13.6 us (4%)
    ppermute x57, starting transfers between devices, send(): return lax.ppermute(value, axis, pairs)  86.5 us
    dot_general x24, matrix products, contract_last(): lax.dot_general(left, right, (((left.ndim - 1,), (right.ndim - 1,)), ((),...  48.6 us
    dynamic_update_slice x28, local copies, waits for them, and re-layouts, pair_up(): both = lax.dynamic_update_slice_in_dim(both, left, first - begin, 1)  42.2 us
    dynamic_update_slice x28, local copies, waits for them, and re-layouts, pair_up(): both = lax.dynamic_update_slice_in_dim(both, right, second - begin, 1)  41.5 us
    dynamic_update_slice x16, local copies, waits for them, and re-layouts, assemble(): whole = lax.dynamic_update_slice_in_dim(whole, piece, offset, 1)  26.7 us
    another operation x36, local copies, waits for them, and re-layouts  21 us
    unnamed x46, local copies, waits for them, and re-layouts  15.3 us
    pallas_call x14, Pallas kernels, local_kernel(): pl.pallas_call(body, out_shape=list(outs), in_specs=specs or [VMEM] * len...  13.6 us
  transfers between devices with their start and end apart: 61, of which 9 were waited for; matrix products, arithmetic and copies ran while one was open for 56% of the time, Pallas kernels for 3%

profile of v15, /device:TPU:0, one launch (start us, length us, event | category | flops | bytes accessed | tf_op | source)
XLA Modules:
  0.0 316.8 jit_solution(11782654178026133048)
XLA Ops:
  2.7 3.1 collective-permute-start
  5.8 2.6 collective-permute-start.1
  9.3 3.5 %collective-permute-start.4 = (f32[64,256]{1,0:T(8,128)}, f32[64,256]{1,0:T(8,128)}, u32[]{:S(2)}, u32[]{:S(2)}) collective-permute-start(f32[64,256]{1,0:T(8,128)} %get-tuple-element.27.refs_0_), channel_id=1, source_target_pairs={{0,2},{1,3},{2,0},{3,1},{4,6},{5,7},{6,4},{7,5},{8,10},{9,11},{10,... | collective-permute-start | bytes 196616 | tf_op jit(solution)/shard_map/ppermute | solution.py:33
  12.8 2.3 shard_map.114
  18.2 4.9 %collective-permute-start.7 = (f32[64,256]{1,0:T(8,128)}, f32[64,256]{1,0:T(8,128)}, u32[]{:S(2)}, u32[]{:S(2)}) collective-permute-start(f32[64,256]{1,0:T(8,128)} %shard_map.115.refs_0_), channel_id=1, source_target_pairs={{0,2},{1,3},{2,0},{3,1},{4,6},{5,7},{6,4},{7,5},{8,10},{9,11},{10,... | collective-permute-start | bytes 196616 | tf_op jit(solution)/shard_map/ppermute | solution.py:33
  27.3 2.0 shard_map.116.refs_1_
  29.3 3.8 %collective-permute-start.13 = (f32[64,256]{1,0:T(8,128)}, f32[64,256]{1,0:T(8,128)}, u32[]{:S(2)}, u32[]{:S(2)}) collective-permute-start(f32[64,256]{1,0:T(8,128)} %shard_map.116.refs_1_), channel_id=1, source_target_pairs={{0,2},{1,3},{2,0},{3,1},{4,6},{5,7},{6,4},{7,5},{8,10},{9,11},{10,... | collective-permute-start | bytes 196616 | tf_op jit(solution)/shard_map/ppermute | solution.py:33
  41.8 2.0 fusion.38
  45.4 2.0 fusion.5
  47.4 3.8 %collective-permute-start.10 = (f32[64,256]{1,0:T(8,128)}, f32[64,256]{1,0:T(8,128)}, u32[]{:S(2)}, u32[]{:S(2)}) collective-permute-start(f32[64,256]{1,0:T(8,128)} %fusion.5), channel_id=1, source_target_pairs={{0,2},{1,3},{2,0},{3,1},{4,6},{5,7},{6,4},{7,5},{8,10},{9,11},{10,... | collective-permute-start | bytes 196616 | tf_op jit(solution)/shard_map/ppermute | solution.py:33
  55.5 2.0 fusion.36
  59.1 2.0 fusion.4
  61.1 3.8 %collective-permute-start.16 = (f32[64,256]{1,0:T(8,128)}, f32[64,256]{1,0:T(8,128)}, u32[]{:S(2)}, u32[]{:S(2)}) collective-permute-start(f32[64,256]{1,0:T(8,128)} %fusion.4), channel_id=1, source_target_pairs={{0,2},{1,3},{2,0},{3,1},{4,6},{5,7},{6,4},{7,5},{8,10},{9,11},{10,... | collective-permute-start | bytes 196616 | tf_op jit(solution)/shard_map/ppermute | solution.py:33
  73.7 2.2 fusion.32
  77.4 2.3 convolution_add_fusion.10.refs_2_
  79.7 3.7 %collective-permute-start.19 = (f32[64,256]{1,0:T(8,128)}, f32[64,256]{1,0:T(8,128)}, u32[]{:S(2)}, u32[]{:S(2)}) collective-permute-start(f32[64,256]{1,0:T(8,128)} %convolution_add_fusion.10.refs_2_), channel_id=1, source_target_pairs={{0,2},{1,3},{2,0},{3,1},{4,6},{5,7},{6,4},{7,5},{8,10},{9,11},{10,... | collective-permute-start | bytes 196616 | tf_op jit(solution)/shard_map/ppermute | solution.py:33
  87.9 2.2 fusion.30
  91.6 2.3 convolution_add_fusion.8.refs_3_
  93.9 3.7 %collective-permute-start.25 = (f32[64,256]{1,0:T(8,128)}, f32[64,256]{1,0:T(8,128)}, u32[]{:S(2)}, u32[]{:S(2)}) collective-permute-start(f32[64,256]{1,0:T(8,128)} %convolution_add_fusion.8.refs_3_), channel_id=1, source_target_pairs={{0,2},{1,3},{2,0},{3,1},{4,6},{5,7},{6,4},{7,5},{8,10},{9,11},{10,... | collective-permute-start | bytes 196616 | tf_op jit(solution)/shard_map/ppermute | solution.py:33
  106.5 2.0 fusion.26
  110.0 2.0 fusion.3
  112.0 3.6 %collective-permute-start.22 = (f32[64,256]{1,0:T(8,128)}, f32[64,256]{1,0:T(8,128)}, u32[]{:S(2)}, u32[]{:S(2)}) collective-permute-start(f32[64,256]{1,0:T(8,128)} %fusion.3), channel_id=1, source_target_pairs={{0,2},{1,3},{2,0},{3,1},{4,6},{5,7},{6,4},{7,5},{8,10},{9,11},{10,... | collective-permute-start | bytes 196616 | tf_op jit(solution)/shard_map/ppermute | solution.py:33
  120.2 2.0 fusion.24
  123.7 2.0 fusion.2
  125.8 3.5 %collective-permute-start.28 = (f32[64,256]{1,0:T(8,128)}, f32[64,256]{1,0:T(8,128)}, u32[]{:S(2)}, u32[]{:S(2)}) collective-permute-start(f32[64,256]{1,0:T(8,128)} %fusion.2), channel_id=1, source_target_pairs={{0,2},{1,3},{2,0},{3,1},{4,6},{5,7},{6,4},{7,5},{8,10},{9,11},{10,... | collective-permute-start | bytes 196616 | tf_op jit(solution)/shard_map/ppermute | solution.py:33
  138.4 2.2 fusion.20
  142.1 2.3 convolution_add_fusion.6.refs_4_
  144.4 3.4 %collective-permute-start.31 = (f32[64,256]{1,0:T(8,128)}, f32[64,256]{1,0:T(8,128)}, u32[]{:S(2)}, u32[]{:S(2)}) collective-permute-start(f32[64,256]{1,0:T(8,128)} %convolution_add_fusion.6.refs_4_), channel_id=1, source_target_pairs={{0,2},{1,3},{2,0},{3,1},{4,6},{5,7},{6,4},{7,5},{8,10},{9,11},{10,... | collective-permute-start | bytes 196616 | tf_op jit(solution)/shard_map/ppermute | solution.py:33
  152.5 2.2 fusion.18
  156.3 2.3 convolution_add_fusion.4.refs_5_
  158.6 3.4 %collective-permute-start.37 = (f32[64,256]{1,0:T(8,128)}, f32[64,256]{1,0:T(8,128)}, u32[]{:S(2)}, u32[]{:S(2)}) collective-permute-start(f32[64,256]{1,0:T(8,128)} %convolution_add_fusion.4.refs_5_), channel_id=1, source_target_pairs={{0,2},{1,3},{2,0},{3,1},{4,6},{5,7},{6,4},{7,5},{8,10},{9,11},{10,... | collective-permute-start | bytes 196616 | tf_op jit(solution)/shard_map/ppermute | solution.py:33
  171.2 2.0 fusion.14
  174.7 2.0 fusion.1
  176.7 3.3 %collective-permute-start.34 = (f32[64,256]{1,0:T(8,128)}, f32[64,256]{1,0:T(8,128)}, u32[]{:S(2)}, u32[]{:S(2)}) collective-permute-start(f32[64,256]{1,0:T(8,128)} %fusion.1), channel_id=1, source_target_pairs={{0,2},{1,3},{2,0},{3,1},{4,6},{5,7},{6,4},{7,5},{8,10},{9,11},{10,... | collective-permute-start | bytes 196616 | tf_op jit(solution)/shard_map/ppermute | solution.py:33
  184.9 2.0 fusion.12
  188.5 2.0 fusion
  190.5 3.3 %collective-permute-start.40 = (f32[64,256]{1,0:T(8,128)}, f32[64,256]{1,0:T(8,128)}, u32[]{:S(2)}, u32[]{:S(2)}) collective-permute-start(f32[64,256]{1,0:T(8,128)} %fusion), channel_id=1, source_target_pairs={{0,2},{1,3},{2,0},{3,1},{4,6},{5,7},{6,4},{7,5},{8,10},{9,11},{10,... | collective-permute-start | bytes 196616 | tf_op jit(solution)/shard_map/ppermute | solution.py:33
  205.0 2.2 collective-permute-start.42
  215.2 1.7 convolution_add_fusion.refs_7_
  218.0 1.8 collective-permute-start.46
  222.0 1.7 dynamic_update_slice.264
  225.8 1.7 dynamic_update_slice.276
  227.6 1.6 dynamic_update_slice.277.refs_1_
  229.9 1.7 dynamic_update_slice.266
  231.6 1.6 dynamic_update_slice.267.refs_1_
  234.0 1.7 dynamic_update_slice.278
  235.7 1.6 dynamic_update_slice.279.refs_2_
  238.1 1.7 dynamic_update_slice.268
  242.1 1.7 dynamic_update_slice.280
  243.8 1.7 dynamic_update_slice.281.refs_3_
  252.2 1.7 dynamic_update_slice.272
  257.6 1.6 dynamic_update_slice.275.refs_3_
  261.5 1.7 dynamic_update_slice.284
  267.0 1.7 dynamic_update_slice.287.refs_4_
  284.4 2.0 shard_map.120
  286.7 2.4 collective-permute-done.51.refs_3_
  289.8 2.8 collective-permute-start.53
  294.4 2.7 collective-permute-done.53.refs_2_
  297.1 1.8 collective-permute-done.54.refs_3_
  299.2 2.1 collective-permute-start.56
  301.3 2.3 collective-permute-start.57
  303.9 2.9 collective-permute-done.57.refs_3_
  307.2 3.0 collective-permute-start.59
  311.9 3.8 %collective-permute-done.60.refs_3_ = f32[16,256]{1,0:T(8,128)S(1)} collective-permute-done((f32[16,256]{1,0:T(8,128)S(1)}, f32[16,256]{1,0:T(8,128)S(1)}, u32[]{:S(2)}, u32[]{:S(2)}) %collective-permute-start.60) | collective-permute-done | bytes 16416 | tf_op jit(solution)/shard_map/ppermute | solution.py:33
  (250 shorter events, 159.9 us)
Async XLA Ops:
  0.6 41.2 %copy-start = (f32[1,3,256,1024]{3,2,1,0:T(8,128)S(1)}, f32[1,3,256,1024]{3,2,1,0:T(8,128)}, u32[]{:S(2)}) copy-start(f32[1,3,256,1024]{3,2,1,0:T(8,128)} %param.12) | copy-start | bytes 9437188
  2.7 10.1 %collective-permute-start = (f32[64,256]{1,0:T(8,128)S(1)}, f32[64,256]{1,0:T(8,128)S(1)}, u32[]{:S(2)}, u32[]{:S(2)}) collective-permute-start(f32[64,256]{1,0:T(8,128)S(1)} %get-tuple-element.24.refs_0_), channel_id=1, source_target_pairs={{0,1},{1,0},{2,3},{3,2},{4,5},{5,4},{6,7},{7,6},{8,9},{9,8},{10,11... | collective-permute-start | bytes 196616 | tf_op jit(solution)/shard_map/ppermute | solution.py:33
  5.8 9.3 %collective-permute-start.1 = (f32[64,256]{1,0:T(8,128)S(1)}, f32[64,256]{1,0:T(8,128)S(1)}, u32[]{:S(2)}, u32[]{:S(2)}) collective-permute-start(f32[64,256]{1,0:T(8,128)S(1)} %get-tuple-element.24.refs_0_), channel_id=1, source_target_pairs={{0,2},{1,3},{2,0},{3,1},{4,6},{5,7},{6,4},{7,5},{8,10},{9,11},{10,... | collective-permute-start | bytes 196616 | tf_op jit(solution)/shard_map/ppermute | solution.py:33
  8.4 6.7 %collective-permute-start.2 = (f32[64,256]{1,0:T(8,128)S(1)}, f32[64,256]{1,0:T(8,128)S(1)}, u32[]{:S(2)}, u32[]{:S(2)}) collective-permute-start(f32[64,256]{1,0:T(8,128)S(1)} %get-tuple-element.24.refs_0_), channel_id=1, source_target_pairs={{0,3},{1,2},{2,1},{3,0},{4,7},{5,6},{6,5},{7,4},{8,11},{9,10},{10,... | collective-permute-start | bytes 196616 | tf_op jit(solution)/shard_map/ppermute | solution.py:33
  8.4 16.7 %collective-permute-start.3 = (f32[64,256]{1,0:T(8,128)}, f32[64,256]{1,0:T(8,128)}, u32[]{:S(2)}, u32[]{:S(2)}) collective-permute-start(f32[64,256]{1,0:T(8,128)} %get-tuple-element.27.refs_0_), channel_id=1, source_target_pairs={{0,1},{1,0},{2,3},{3,2},{4,5},{5,4},{6,7},{7,6},{8,9},{9,8},{10,11... | collective-permute-start | bytes 196616 | tf_op jit(solution)/shard_map/ppermute | solution.py:33
  9.3 16.0 %collective-permute-start.4 = (f32[64,256]{1,0:T(8,128)}, f32[64,256]{1,0:T(8,128)}, u32[]{:S(2)}, u32[]{:S(2)}) collective-permute-start(f32[64,256]{1,0:T(8,128)} %get-tuple-element.27.refs_0_), channel_id=1, source_target_pairs={{0,2},{1,3},{2,0},{3,1},{4,6},{5,7},{6,4},{7,5},{8,10},{9,11},{10,... | collective-permute-start | bytes 196616 | tf_op jit(solution)/shard_map/ppermute | solution.py:33
  12.8 12.5 %collective-permute-start.5 = (f32[64,256]{1,0:T(8,128)}, f32[64,256]{1,0:T(8,128)}, u32[]{:S(2)}, u32[]{:S(2)}) collective-permute-start(f32[64,256]{1,0:T(8,128)} %get-tuple-element.27.refs_0_), channel_id=1, source_target_pairs={{0,3},{1,2},{2,1},{3,0},{4,7},{5,6},{6,5},{7,4},{8,11},{9,10},{10,... | collective-permute-start | bytes 196616 | tf_op jit(solution)/shard_map/ppermute | solution.py:33
  18.2 19.8 %collective-permute-start.7 = (f32[64,256]{1,0:T(8,128)}, f32[64,256]{1,0:T(8,128)}, u32[]{:S(2)}, u32[]{:S(2)}) collective-permute-start(f32[64,256]{1,0:T(8,128)} %shard_map.115.refs_0_), channel_id=1, source_target_pairs={{0,2},{1,3},{2,0},{3,1},{4,6},{5,7},{6,4},{7,5},{8,10},{9,11},{10,... | collective-permute-start | bytes 196616 | tf_op jit(solution)/shard_map/ppermute | solution.py:33
  23.2 17.1 %collective-permute-start.8 = (f32[64,256]{1,0:T(8,128)}, f32[64,256]{1,0:T(8,128)}, u32[]{:S(2)}, u32[]{:S(2)}) collective-permute-start(f32[64,256]{1,0:T(8,128)} %shard_map.115.refs_0_), channel_id=1, source_target_pairs={{0,3},{1,2},{2,1},{3,0},{4,7},{5,6},{6,5},{7,4},{8,11},{9,10},{10,... | collective-permute-start | bytes 196616 | tf_op jit(solution)/shard_map/ppermute | solution.py:33
  25.1 18.8 %collective-permute-start.6 = (f32[64,256]{1,0:T(8,128)}, f32[64,256]{1,0:T(8,128)}, u32[]{:S(2)}, u32[]{:S(2)}) collective-permute-start(f32[64,256]{1,0:T(8,128)} %shard_map.115.refs_0_), channel_id=1, source_target_pairs={{0,1},{1,0},{2,3},{3,2},{4,5},{5,4},{6,7},{7,6},{8,9},{9,8},{10,11... | collective-permute-start | bytes 196616 | tf_op jit(solution)/shard_map/ppermute | solution.py:33
  29.3 22.4 %collective-permute-start.13 = (f32[64,256]{1,0:T(8,128)}, f32[64,256]{1,0:T(8,128)}, u32[]{:S(2)}, u32[]{:S(2)}) collective-permute-start(f32[64,256]{1,0:T(8,128)} %shard_map.116.refs_1_), channel_id=1, source_target_pairs={{0,2},{1,3},{2,0},{3,1},{4,6},{5,7},{6,4},{7,5},{8,10},{9,11},{10,... | collective-permute-start | bytes 196616 | tf_op jit(solution)/shard_map/ppermute | solution.py:33
  33.2 20.9 %collective-permute-start.14 = (f32[64,256]{1,0:T(8,128)}, f32[64,256]{1,0:T(8,128)}, u32[]{:S(2)}, u32[]{:S(2)}) collective-permute-start(f32[64,256]{1,0:T(8,128)} %shard_map.116.refs_1_), channel_id=1, source_target_pairs={{0,3},{1,2},{2,1},{3,0},{4,7},{5,6},{6,5},{7,4},{8,11},{9,10},{10,... | collective-permute-start | bytes 196616 | tf_op jit(solution)/shard_map/ppermute | solution.py:33
  38.0 19.5 %collective-permute-start.12 = (f32[64,256]{1,0:T(8,128)}, f32[64,256]{1,0:T(8,128)}, u32[]{:S(2)}, u32[]{:S(2)}) collective-permute-start(f32[64,256]{1,0:T(8,128)} %shard_map.116.refs_1_), channel_id=1, source_target_pairs={{0,1},{1,0},{2,3},{3,2},{4,5},{5,4},{6,7},{7,6},{8,9},{9,8},{10,11... | collective-permute-start | bytes 196616 | tf_op jit(solution)/shard_map/ppermute | solution.py:33
  47.4 22.5 %collective-permute-start.10 = (f32[64,256]{1,0:T(8,128)}, f32[64,256]{1,0:T(8,128)}, u32[]{:S(2)}, u32[]{:S(2)}) collective-permute-start(f32[64,256]{1,0:T(8,128)} %fusion.5), channel_id=1, source_target_pairs={{0,2},{1,3},{2,0},{3,1},{4,6},{5,7},{6,4},{7,5},{8,10},{9,11},{10,... | collective-permute-start | bytes 196616 | tf_op jit(solution)/shard_map/ppermute | solution.py:33
  51.2 20.9 %collective-permute-start.11 = (f32[64,256]{1,0:T(8,128)}, f32[64,256]{1,0:T(8,128)}, u32[]{:S(2)}, u32[]{:S(2)}) collective-permute-start(f32[64,256]{1,0:T(8,128)} %fusion.5), channel_id=1, source_target_pairs={{0,3},{1,2},{2,1},{3,0},{4,7},{5,6},{6,5},{7,4},{8,11},{9,10},{10,... | collective-permute-start | bytes 196616 | tf_op jit(solution)/shard_map/ppermute | solution.py:33
  51.8 24.1 %collective-permute-start.9 = (f32[64,256]{1,0:T(8,128)}, f32[64,256]{1,0:T(8,128)}, u32[]{:S(2)}, u32[]{:S(2)}) collective-permute-start(f32[64,256]{1,0:T(8,128)} %fusion.5), channel_id=1, source_target_pairs={{0,1},{1,0},{2,3},{3,2},{4,5},{5,4},{6,7},{7,6},{8,9},{9,8},{10,11... | collective-permute-start | bytes 196616 | tf_op jit(solution)/shard_map/ppermute | solution.py:33
  61.1 23.0 %collective-permute-start.16 = (f32[64,256]{1,0:T(8,128)}, f32[64,256]{1,0:T(8,128)}, u32[]{:S(2)}, u32[]{:S(2)}) collective-permute-start(f32[64,256]{1,0:T(8,128)} %fusion.4), channel_id=1, source_target_pairs={{0,2},{1,3},{2,0},{3,1},{4,6},{5,7},{6,4},{7,5},{8,10},{9,11},{10,... | collective-permute-start | bytes 196616 | tf_op jit(solution)/shard_map/ppermute | solution.py:33
  64.9 21.4 %collective-permute-start.17 = (f32[64,256]{1,0:T(8,128)}, f32[64,256]{1,0:T(8,128)}, u32[]{:S(2)}, u32[]{:S(2)}) collective-permute-start(f32[64,256]{1,0:T(8,128)} %fusion.4), channel_id=1, source_target_pairs={{0,3},{1,2},{2,1},{3,0},{4,7},{5,6},{6,5},{7,4},{8,11},{9,10},{10,... | collective-permute-start | bytes 196616 | tf_op jit(solution)/shard_map/ppermute | solution.py:33
  69.9 20.2 %collective-permute-start.15 = (f32[64,256]{1,0:T(8,128)}, f32[64,256]{1,0:T(8,128)}, u32[]{:S(2)}, u32[]{:S(2)}) collective-permute-start(f32[64,256]{1,0:T(8,128)} %fusion.4), channel_id=1, source_target_pairs={{0,1},{1,0},{2,3},{3,2},{4,5},{5,4},{6,7},{7,6},{8,9},{9,8},{10,11... | collective-permute-start | bytes 196616 | tf_op jit(solution)/shard_map/ppermute | solution.py:33
  79.7 23.0 %collective-permute-start.19 = (f32[64,256]{1,0:T(8,128)}, f32[64,256]{1,0:T(8,128)}, u32[]{:S(2)}, u32[]{:S(2)}) collective-permute-start(f32[64,256]{1,0:T(8,128)} %convolution_add_fusion.10.refs_2_), channel_id=1, source_target_pairs={{0,2},{1,3},{2,0},{3,1},{4,6},{5,7},{6,4},{7,5},{8,10},{9,11},{10,... | collective-permute-start | bytes 196616 | tf_op jit(solution)/shard_map/ppermute | solution.py:33
  83.4 21.5 %collective-permute-start.20 = (f32[64,256]{1,0:T(8,128)}, f32[64,256]{1,0:T(8,128)}, u32[]{:S(2)}, u32[]{:S(2)}) collective-permute-start(f32[64,256]{1,0:T(8,128)} %convolution_add_fusion.10.refs_2_), channel_id=1, source_target_pairs={{0,3},{1,2},{2,1},{3,0},{4,7},{5,6},{6,5},{7,4},{8,11},{9,10},{10,... | collective-permute-start | bytes 196616 | tf_op jit(solution)/shard_map/ppermute | solution.py:33
  84.1 24.4 %collective-permute-start.18 = (f32[64,256]{1,0:T(8,128)}, f32[64,256]{1,0:T(8,128)}, u32[]{:S(2)}, u32[]{:S(2)}) collective-permute-start(f32[64,256]{1,0:T(8,128)} %convolution_add_fusion.10.refs_2_), channel_id=1, source_target_pairs={{0,1},{1,0},{2,3},{3,2},{4,5},{5,4},{6,7},{7,6},{8,9},{9,8},{10,11... | collective-permute-start | bytes 196616 | tf_op jit(solution)/shard_map/ppermute | solution.py:33
  93.9 22.6 %collective-permute-start.25 = (f32[64,256]{1,0:T(8,128)}, f32[64,256]{1,0:T(8,128)}, u32[]{:S(2)}, u32[]{:S(2)}) collective-permute-start(f32[64,256]{1,0:T(8,128)} %convolution_add_fusion.8.refs_3_), channel_id=1, source_target_pairs={{0,2},{1,3},{2,0},{3,1},{4,6},{5,7},{6,4},{7,5},{8,10},{9,11},{10,... | collective-permute-start | bytes 196616 | tf_op jit(solution)/shard_map/ppermute | solution.py:33
  97.6 21.1 %collective-permute-start.26 = (f32[64,256]{1,0:T(8,128)}, f32[64,256]{1,0:T(8,128)}, u32[]{:S(2)}, u32[]{:S(2)}) collective-permute-start(f32[64,256]{1,0:T(8,128)} %convolution_add_fusion.8.refs_3_), channel_id=1, source_target_pairs={{0,3},{1,2},{2,1},{3,0},{4,7},{5,6},{6,5},{7,4},{8,11},{9,10},{10,... | collective-permute-start | bytes 196616 | tf_op jit(solution)/shard_map/ppermute | solution.py:33
  102.7 19.5 %collective-permute-start.24 = (f32[64,256]{1,0:T(8,128)}, f32[64,256]{1,0:T(8,128)}, u32[]{:S(2)}, u32[]{:S(2)}) collective-permute-start(f32[64,256]{1,0:T(8,128)} %convolution_add_fusion.8.refs_3_), channel_id=1, source_target_pairs={{0,1},{1,0},{2,3},{3,2},{4,5},{5,4},{6,7},{7,6},{8,9},{9,8},{10,11... | collective-permute-start | bytes 196616 | tf_op jit(solution)/shard_map/ppermute | solution.py:33
  112.0 22.6 %collective-permute-start.22 = (f32[64,256]{1,0:T(8,128)}, f32[64,256]{1,0:T(8,128)}, u32[]{:S(2)}, u32[]{:S(2)}) collective-permute-start(f32[64,256]{1,0:T(8,128)} %fusion.3), channel_id=1, source_target_pairs={{0,2},{1,3},{2,0},{3,1},{4,6},{5,7},{6,4},{7,5},{8,10},{9,11},{10,... | collective-permute-start | bytes 196616 | tf_op jit(solution)/shard_map/ppermute | solution.py:33
  115.6 21.2 %collective-permute-start.23 = (f32[64,256]{1,0:T(8,128)}, f32[64,256]{1,0:T(8,128)}, u32[]{:S(2)}, u32[]{:S(2)}) collective-permute-start(f32[64,256]{1,0:T(8,128)} %fusion.3), channel_id=1, source_target_pairs={{0,3},{1,2},{2,1},{3,0},{4,7},{5,6},{6,5},{7,4},{8,11},{9,10},{10,... | collective-permute-start | bytes 196616 | tf_op jit(solution)/shard_map/ppermute | solution.py:33
  116.5 24.1 %collective-permute-start.21 = (f32[64,256]{1,0:T(8,128)}, f32[64,256]{1,0:T(8,128)}, u32[]{:S(2)}, u32[]{:S(2)}) collective-permute-start(f32[64,256]{1,0:T(8,128)} %fusion.3), channel_id=1, source_target_pairs={{0,1},{1,0},{2,3},{3,2},{4,5},{5,4},{6,7},{7,6},{8,9},{9,8},{10,11... | collective-permute-start | bytes 196616 | tf_op jit(solution)/shard_map/ppermute | solution.py:33
  125.8 23.0 %collective-permute-start.28 = (f32[64,256]{1,0:T(8,128)}, f32[64,256]{1,0:T(8,128)}, u32[]{:S(2)}, u32[]{:S(2)}) collective-permute-start(f32[64,256]{1,0:T(8,128)} %fusion.2), channel_id=1, source_target_pairs={{0,2},{1,3},{2,0},{3,1},{4,6},{5,7},{6,4},{7,5},{8,10},{9,11},{10,... | collective-permute-start | bytes 196616 | tf_op jit(solution)/shard_map/ppermute | solution.py:33
  129.3 21.7 %collective-permute-start.29 = (f32[64,256]{1,0:T(8,128)}, f32[64,256]{1,0:T(8,128)}, u32[]{:S(2)}, u32[]{:S(2)}) collective-permute-start(f32[64,256]{1,0:T(8,128)} %fusion.2), channel_id=1, source_target_pairs={{0,3},{1,2},{2,1},{3,0},{4,7},{5,6},{6,5},{7,4},{8,11},{9,10},{10,... | collective-permute-start | bytes 196616 | tf_op jit(solution)/shard_map/ppermute | solution.py:33
  134.6 20.2 %collective-permute-start.27 = (f32[64,256]{1,0:T(8,128)}, f32[64,256]{1,0:T(8,128)}, u32[]{:S(2)}, u32[]{:S(2)}) collective-permute-start(f32[64,256]{1,0:T(8,128)} %fusion.2), channel_id=1, source_target_pairs={{0,1},{1,0},{2,3},{3,2},{4,5},{5,4},{6,7},{7,6},{8,9},{9,8},{10,11... | collective-permute-start | bytes 196616 | tf_op jit(solution)/shard_map/ppermute | solution.py:33
  144.4 23.1 %collective-permute-start.31 = (f32[64,256]{1,0:T(8,128)}, f32[64,256]{1,0:T(8,128)}, u32[]{:S(2)}, u32[]{:S(2)}) collective-permute-start(f32[64,256]{1,0:T(8,128)} %convolution_add_fusion.6.refs_4_), channel_id=1, source_target_pairs={{0,2},{1,3},{2,0},{3,1},{4,6},{5,7},{6,4},{7,5},{8,10},{9,11},{10,... | collective-permute-start | bytes 196616 | tf_op jit(solution)/shard_map/ppermute | solution.py:33
  147.8 21.8 %collective-permute-start.32 = (f32[64,256]{1,0:T(8,128)}, f32[64,256]{1,0:T(8,128)}, u32[]{:S(2)}, u32[]{:S(2)}) collective-permute-start(f32[64,256]{1,0:T(8,128)} %convolution_add_fusion.6.refs_4_), channel_id=1, source_target_pairs={{0,3},{1,2},{2,1},{3,0},{4,7},{5,6},{6,5},{7,4},{8,11},{9,10},{10,... | collective-permute-start | bytes 196616 | tf_op jit(solution)/shard_map/ppermute | solution.py:33
  148.8 24.4 %collective-permute-start.30 = (f32[64,256]{1,0:T(8,128)}, f32[64,256]{1,0:T(8,128)}, u32[]{:S(2)}, u32[]{:S(2)}) collective-permute-start(f32[64,256]{1,0:T(8,128)} %convolution_add_fusion.6.refs_4_), channel_id=1, source_target_pairs={{0,1},{1,0},{2,3},{3,2},{4,5},{5,4},{6,7},{7,6},{8,9},{9,8},{10,11... | collective-permute-start | bytes 196616 | tf_op jit(solution)/shard_map/ppermute | solution.py:33
  158.6 22.6 %collective-permute-start.37 = (f32[64,256]{1,0:T(8,128)}, f32[64,256]{1,0:T(8,128)}, u32[]{:S(2)}, u32[]{:S(2)}) collective-permute-start(f32[64,256]{1,0:T(8,128)} %convolution_add_fusion.4.refs_5_), channel_id=1, source_target_pairs={{0,2},{1,3},{2,0},{3,1},{4,6},{5,7},{6,4},{7,5},{8,10},{9,11},{10,... | collective-permute-start | bytes 196616 | tf_op jit(solution)/shard_map/ppermute | solution.py:33
  162.0 21.4 %collective-permute-start.38 = (f32[64,256]{1,0:T(8,128)}, f32[64,256]{1,0:T(8,128)}, u32[]{:S(2)}, u32[]{:S(2)}) collective-permute-start(f32[64,256]{1,0:T(8,128)} %convolution_add_fusion.4.refs_5_), channel_id=1, source_target_pairs={{0,3},{1,2},{2,1},{3,0},{4,7},{5,6},{6,5},{7,4},{8,11},{9,10},{10,... | collective-permute-start | bytes 196616 | tf_op jit(solution)/shard_map/ppermute | solution.py:33
  167.4 19.5 %collective-permute-start.36 = (f32[64,256]{1,0:T(8,128)}, f32[64,256]{1,0:T(8,128)}, u32[]{:S(2)}, u32[]{:S(2)}) collective-permute-start(f32[64,256]{1,0:T(8,128)} %convolution_add_fusion.4.refs_5_), channel_id=1, source_target_pairs={{0,1},{1,0},{2,3},{3,2},{4,5},{5,4},{6,7},{7,6},{8,9},{9,8},{10,11... | collective-permute-start | bytes 196616 | tf_op jit(solution)/shard_map/ppermute | solution.py:33
  176.7 20.8 %collective-permute-start.34 = (f32[64,256]{1,0:T(8,128)}, f32[64,256]{1,0:T(8,128)}, u32[]{:S(2)}, u32[]{:S(2)}) collective-permute-start(f32[64,256]{1,0:T(8,128)} %fusion.1), channel_id=1, source_target_pairs={{0,2},{1,3},{2,0},{3,1},{4,6},{5,7},{6,4},{7,5},{8,10},{9,11},{10,... | collective-permute-start | bytes 196616 | tf_op jit(solution)/shard_map/ppermute | solution.py:33
  180.0 19.5 %collective-permute-start.35 = (f32[64,256]{1,0:T(8,128)}, f32[64,256]{1,0:T(8,128)}, u32[]{:S(2)}, u32[]{:S(2)}) collective-permute-start(f32[64,256]{1,0:T(8,128)} %fusion.1), channel_id=1, source_target_pairs={{0,3},{1,2},{2,1},{3,0},{4,7},{5,6},{6,5},{7,4},{8,11},{9,10},{10,... | collective-permute-start | bytes 196616 | tf_op jit(solution)/shard_map/ppermute | solution.py:33
  181.2 21.0 %collective-permute-start.33 = (f32[64,256]{1,0:T(8,128)}, f32[64,256]{1,0:T(8,128)}, u32[]{:S(2)}, u32[]{:S(2)}) collective-permute-start(f32[64,256]{1,0:T(8,128)} %fusion.1), channel_id=1, source_target_pairs={{0,1},{1,0},{2,3},{3,2},{4,5},{5,4},{6,7},{7,6},{8,9},{9,8},{10,11... | collective-permute-start | bytes 196616 | tf_op jit(solution)/shard_map/ppermute | solution.py:33
  190.5 17.6 %collective-permute-start.40 = (f32[64,256]{1,0:T(8,128)}, f32[64,256]{1,0:T(8,128)}, u32[]{:S(2)}, u32[]{:S(2)}) collective-permute-start(f32[64,256]{1,0:T(8,128)} %fusion), channel_id=1, source_target_pairs={{0,2},{1,3},{2,0},{3,1},{4,6},{5,7},{6,4},{7,5},{8,10},{9,11},{10,... | collective-permute-start | bytes 196616 | tf_op jit(solution)/shard_map/ppermute | solution.py:33
  193.8 17.2 %collective-permute-start.41 = (f32[64,256]{1,0:T(8,128)}, f32[64,256]{1,0:T(8,128)}, u32[]{:S(2)}, u32[]{:S(2)}) collective-permute-start(f32[64,256]{1,0:T(8,128)} %fusion), channel_id=1, source_target_pairs={{0,3},{1,2},{2,1},{3,0},{4,7},{5,6},{6,5},{7,4},{8,11},{9,10},{10,... | collective-permute-start | bytes 196616 | tf_op jit(solution)/shard_map/ppermute | solution.py:33
  198.2 15.5 %collective-permute-start.39 = (f32[64,256]{1,0:T(8,128)}, f32[64,256]{1,0:T(8,128)}, u32[]{:S(2)}, u32[]{:S(2)}) collective-permute-start(f32[64,256]{1,0:T(8,128)} %fusion), channel_id=1, source_target_pairs={{0,1},{1,0},{2,3},{3,2},{4,5},{5,4},{6,7},{7,6},{8,9},{9,8},{10,11... | collective-permute-start | bytes 196616 | tf_op jit(solution)/shard_map/ppermute | solution.py:33
  205.0 14.9 %collective-permute-start.42 = (f32[64,256]{1,0:T(8,128)S(1)}, f32[64,256]{1,0:T(8,128)S(1)}, u32[]{:S(2)}, u32[]{:S(2)}) collective-permute-start(f32[64,256]{1,0:T(8,128)S(1)} %convolution_add_fusion.2.refs_6_), channel_id=1, source_target_pairs={{0,1},{1,0},{2,3},{3,2},{4,5},{5,4},{6,7},{7,6},{8,9},{9,8},{10,11... | collective-permute-start | bytes 196616 | tf_op jit(solution)/shard_map/ppermute | solution.py:33
  207.2 46.7 %collective-permute-start.43 = (f32[64,256]{1,0:T(8,128)S(1)}, f32[64,256]{1,0:T(8,128)}, u32[]{:S(2)}, u32[]{:S(2)}) collective-permute-start(f32[64,256]{1,0:T(8,128)S(1)} %convolution_add_fusion.2.refs_6_), channel_id=1, source_target_pairs={{0,2},{1,3},{2,0},{3,1},{4,6},{5,7},{6,4},{7,5},{8,10},{9,11},{10,... | collective-permute-start | bytes 196616 | tf_op jit(solution)/shard_map/ppermute | solution.py:33
  208.1 48.0 %collective-permute-start.44 = (f32[64,256]{1,0:T(8,128)S(1)}, f32[64,256]{1,0:T(8,128)}, u32[]{:S(2)}, u32[]{:S(2)}) collective-permute-start(f32[64,256]{1,0:T(8,128)S(1)} %convolution_add_fusion.2.refs_6_), channel_id=1, source_target_pairs={{0,3},{1,2},{2,1},{3,0},{4,7},{5,6},{6,5},{7,4},{8,11},{9,10},{10,... | collective-permute-start | bytes 196616 | tf_op jit(solution)/shard_map/ppermute | solution.py:33
  216.8 42.5 %collective-permute-start.45 = (f32[64,256]{1,0:T(8,128)S(1)}, f32[64,256]{1,0:T(8,128)}, u32[]{:S(2)}, u32[]{:S(2)}) collective-permute-start(f32[64,256]{1,0:T(8,128)S(1)} %convolution_add_fusion.refs_7_), channel_id=1, source_target_pairs={{0,1},{1,0},{2,3},{3,2},{4,5},{5,4},{6,7},{7,6},{8,9},{9,8},{10,11... | collective-permute-start | bytes 196616 | tf_op jit(solution)/shard_map/ppermute | solution.py:33
  218.0 45.3 %collective-permute-start.46 = (f32[64,256]{1,0:T(8,128)S(1)}, f32[64,256]{1,0:T(8,128)}, u32[]{:S(2)}, u32[]{:S(2)}) collective-permute-start(f32[64,256]{1,0:T(8,128)S(1)} %convolution_add_fusion.refs_7_), channel_id=1, source_target_pairs={{0,2},{1,3},{2,0},{3,1},{4,6},{5,7},{6,4},{7,5},{8,10},{9,11},{10,... | collective-permute-start | bytes 196616 | tf_op jit(solution)/shard_map/ppermute | solution.py:33
  219.8 45.7 %collective-permute-start.47 = (f32[64,256]{1,0:T(8,128)S(1)}, f32[64,256]{1,0:T(8,128)}, u32[]{:S(2)}, u32[]{:S(2)}) collective-permute-start(f32[64,256]{1,0:T(8,128)S(1)} %convolution_add_fusion.refs_7_), channel_id=1, source_target_pairs={{0,3},{1,2},{2,1},{3,0},{4,7},{5,6},{6,5},{7,4},{8,11},{9,10},{10,... | collective-permute-start | bytes 196616 | tf_op jit(solution)/shard_map/ppermute | solution.py:33
  229.2 39.5 %copy-start.19 = (s32[1,1,3]{2,1,0:T(1,128)S(1)}, s32[1,1,3]{2,1,0:T(1,128)}, u32[]{:S(2)}) copy-start(s32[1,1,3]{2,1,0:T(1,128)} %refs_6_.1) | copy-start | bytes 40
  242.1 32.1 %copy-start.20 = (s32[1,1,3]{2,1,0:T(1,128)S(1)}, s32[1,1,3]{2,1,0:T(1,128)}, u32[]{:S(2)}) copy-start(s32[1,1,3]{2,1,0:T(1,128)} %refs_7_.1) | copy-start | bytes 40
  279.4 1.4 collective-permute-start.48
  280.9 5.5 %collective-permute-start.49 = (f32[2,16,512]{2,1,0:T(8,128)S(1)}, f32[2,16,512]{2,1,0:T(8,128)S(1)}, u32[]{:S(2)}, u32[]{:S(2)}) collective-permute-start(f32[2,16,512]{2,1,0:T(8,128)S(1)} %get-tuple-element.32), channel_id=1, source_target_pairs={{0,8},{4,12},{8,0},{12,4},{16,24},{20,28},{24,16},{28,20},{1,9},{5... | collective-permute-start | bytes 196616 | tf_op jit(solution)/shard_map/ppermute | solution.py:87
  282.4 4.3 %collective-permute-start.50 = (f32[2,16,512]{2,1,0:T(8,128)S(1)}, f32[2,16,512]{2,1,0:T(8,128)S(1)}, u32[]{:S(2)}, u32[]{:S(2)}) collective-permute-start(f32[2,16,512]{2,1,0:T(8,128)S(1)} %get-tuple-element.33), channel_id=1, source_target_pairs={{0,16},{4,20},{8,24},{12,28},{16,0},{20,4},{24,8},{28,12},{1,17},{... | collective-permute-start | bytes 196616 | tf_op jit(solution)/shard_map/ppermute | solution.py:87
  283.9 5.2 %collective-permute-start.51 = (f32[2,16,512]{2,1,0:T(8,128)S(1)}, f32[2,16,512]{2,1,0:T(8,128)S(1)}, u32[]{:S(2)}, u32[]{:S(2)}) collective-permute-start(f32[2,16,512]{2,1,0:T(8,128)S(1)} %get-tuple-element.34), channel_id=1, source_target_pairs={{0,24},{4,28},{8,16},{12,20},{16,8},{20,12},{24,0},{28,4},{1,25},{... | collective-permute-start | bytes 196616 | tf_op jit(solution)/shard_map/ppermute | solution.py:87
  289.5 4.9 %collective-permute-start.52 = (f32[16,1280]{1,0:T(8,128)S(1)}, f32[16,1280]{1,0:T(8,128)S(1)}, u32[]{:S(2)}, u32[]{:S(2)}) collective-permute-start(f32[16,1280]{1,0:T(8,128)S(1)} %get-tuple-element.37), channel_id=1, source_target_pairs={{0,1},{1,0},{2,3},{3,2},{4,5},{5,4},{6,7},{7,6},{8,9},{9,8},{10,11... | collective-permute-start | bytes 245768 | tf_op jit(solution)/shard_map/ppermute | solution.py:33
  289.8 7.3 %collective-permute-start.53 = (f32[16,1280]{1,0:T(8,128)S(1)}, f32[16,1280]{1,0:T(8,128)S(1)}, u32[]{:S(2)}, u32[]{:S(2)}) collective-permute-start(f32[16,1280]{1,0:T(8,128)S(1)} %get-tuple-element.38), channel_id=1, source_target_pairs={{0,2},{1,3},{2,0},{3,1},{4,6},{5,7},{6,4},{7,5},{8,10},{9,11},{10,... | collective-permute-start | bytes 245768 | tf_op jit(solution)/shard_map/ppermute | solution.py:33
  292.5 6.3 %collective-permute-start.54 = (f32[16,1280]{1,0:T(8,128)S(1)}, f32[16,1280]{1,0:T(8,128)S(1)}, u32[]{:S(2)}, u32[]{:S(2)}) collective-permute-start(f32[16,1280]{1,0:T(8,128)S(1)} %get-tuple-element.39), channel_id=1, source_target_pairs={{0,3},{1,2},{2,1},{3,0},{4,7},{5,6},{6,5},{7,4},{8,11},{9,10},{10,... | collective-permute-start | bytes 245768 | tf_op jit(solution)/shard_map/ppermute | solution.py:33
  299.2 4.4 %collective-permute-start.55 = (f32[16,256]{1,0:T(8,128)S(1)}, f32[16,256]{1,0:T(8,128)S(1)}, u32[]{:S(2)}, u32[]{:S(2)}) collective-permute-start(f32[16,256]{1,0:T(8,128)S(1)} %get-tuple-element.42.refs_0_.refs_6_), channel_id=1, source_target_pairs={{0,1},{1,0},{2,3},{3,2},{4,5},{5,4},{6,7},{7,6},{8,9},{9,8},{10,11... | collective-permute-start | bytes 49160 | tf_op jit(solution)/shard_map/ppermute | solution.py:33
  299.2 4.7 %collective-permute-start.56 = (f32[16,256]{1,0:T(8,128)S(1)}, f32[16,256]{1,0:T(8,128)S(1)}, u32[]{:S(2)}, u32[]{:S(2)}) collective-permute-start(f32[16,256]{1,0:T(8,128)S(1)} %get-tuple-element.42.refs_0_.refs_6_), channel_id=1, source_target_pairs={{0,2},{1,3},{2,0},{3,1},{4,6},{5,7},{6,4},{7,5},{8,10},{9,11},{10,... | collective-permute-start | bytes 49160 | tf_op jit(solution)/shard_map/ppermute | solution.py:33
  301.3 5.5 %collective-permute-start.57 = (f32[16,256]{1,0:T(8,128)S(1)}, f32[16,256]{1,0:T(8,128)S(1)}, u32[]{:S(2)}, u32[]{:S(2)}) collective-permute-start(f32[16,256]{1,0:T(8,128)S(1)} %get-tuple-element.42.refs_0_.refs_6_), channel_id=1, source_target_pairs={{0,3},{1,2},{2,1},{3,0},{4,7},{5,6},{6,5},{7,4},{8,11},{9,10},{10,... | collective-permute-start | bytes 49160 | tf_op jit(solution)/shard_map/ppermute | solution.py:33
  307.2 4.4 %collective-permute-start.58 = (f32[16,256]{1,0:T(8,128)S(1)}, f32[16,256]{1,0:T(8,128)S(1)}, u32[]{:S(2)}, u32[]{:S(2)}) collective-permute-start(f32[16,256]{1,0:T(8,128)S(1)} %shard_map.125.refs_0_), channel_id=1, source_target_pairs={{0,1},{1,0},{2,3},{3,2},{4,5},{5,4},{6,7},{7,6},{8,9},{9,8},{10,11... | collective-permute-start | bytes 49160 | tf_op jit(solution)/shard_map/ppermute | solution.py:33
  307.2 4.7 %collective-permute-start.59 = (f32[16,256]{1,0:T(8,128)S(1)}, f32[16,256]{1,0:T(8,128)S(1)}, u32[]{:S(2)}, u32[]{:S(2)}) collective-permute-start(f32[16,256]{1,0:T(8,128)S(1)} %shard_map.125.refs_0_), channel_id=1, source_target_pairs={{0,2},{1,3},{2,0},{3,1},{4,6},{5,7},{6,4},{7,5},{8,10},{9,11},{10,... | collective-permute-start | bytes 49160 | tf_op jit(solution)/shard_map/ppermute | solution.py:33
  310.2 5.5 %collective-permute-start.60 = (f32[16,256]{1,0:T(8,128)S(1)}, f32[16,256]{1,0:T(8,128)S(1)}, u32[]{:S(2)}, u32[]{:S(2)}) collective-permute-start(f32[16,256]{1,0:T(8,128)S(1)} %shard_map.125.refs_0_), channel_id=1, source_target_pairs={{0,3},{1,2},{2,1},{3,0},{4,7},{5,6},{6,5},{7,4},{8,11},{9,10},{10,... | collective-permute-start | bytes 49160 | tf_op jit(solution)/shard_map/ppermute | solution.py:33
  (20 other events, 70.9 us)

commit v16 on v14

--- a/solution.py
+++ b/solution.py
@@ -33,14 +33,17 @@
     return lax.ppermute(value, axis, pairs)
 
 
-def gather_rows(value):
+def gather_rows(value, ties=()):
     members = lax.axis_size("grp")
     me = lax.axis_index("grp")
     rows = value.shape[1]
     pieces = [(me * rows, value)]
     for distance in range(1, members):
         owner = partner(me, distance, members)
-        pieces.append((owner * rows, send(value, "grp", distance)))
+        tied = value
+        if distance in dict(ties):
+            tied = lax.optimization_barrier((value, dict(ties)[distance]))[0]
+        pieces.append((owner * rows, send(tied, "grp", distance)))
     return pieces
 
 
@@ -385,36 +388,6 @@
         whole[:, j * width : (j + 1) * width] = value
 
 
-def apply_first(value, factor):
-    members = lax.axis_size("grp")
-    depth, width = value.shape
-    rows, order = factor.shape[2:]
-    held = [value] + [send(value, "grp", distance) for distance in range(1, members)]
-
-    def body(*refs):
-        factor_ref, out, whole, matrix, sem = refs[members:]
-        copy = pltpu.make_async_copy(factor_ref.at[0, 0], matrix, sem)
-        copy.start()
-        put_in_order([refs[d][...] for d in range(members)], whole)
-        copy.wait()
-        top, rest = high_low(matrix[...])
-        out[...] = split_product(whole[...], top, rest)
-
-    return local_kernel(
-        body,
-        [float_array(depth, rows)],
-        [*held, factor],
-        [VMEM] * members + [ANY],
-        flops=6 * depth * rows * order,
-        scratch=[
-            pltpu.VMEM((depth, order), jnp.float32),
-            pltpu.VMEM((rows, order), jnp.float32),
-            pltpu.SemaphoreType.DMA(()),
-        ],
-        limit=56 * 2**20,
-    )[0]
-
-
 def apply_split(pieces, top, rest, index, base=None, begin=0, others=None):
     members = lax.axis_size("grp")
     part, width = pieces[0].shape
@@ -466,24 +439,33 @@
     streams = 2 if rhs_count % 16 == 0 else 1
     residuals = turn_first(rhs_local, streams)
     later = turn(rhs_local, 1, supernodes, streams)
-    solved = []
-    gathered = []
-    for current in range(supernodes):
-        owned = []
-        for residual in residuals:
-            if current:
-                pieces = gather_rows(residual)
-                owned.append(apply_pieces(diag_inv_local, current, pieces))
+    first = diag_inv_local[0, 0]
+    rounded = lax.reduce_precision(first, 8, 7)
+    first_top = rounded.astype(jnp.bfloat16)[None]
+    first_rest = (first - rounded).astype(jnp.bfloat16)[None]
+    solved = [[None] * streams for _ in range(supernodes)]
+    gathered = [[None] * streams for _ in range(supernodes)]
+    values = list(residuals)
+    last = None
+    for step in range(2 * supernodes):
+        current = step // 2
+        for i in range(streams):
+            ties = [(1, last[1][1])] if last is not None else []
+            pieces = gather_rows(values[i], ties)
+            if step == 0:
+                owned = apply_split([p for _, p in pieces], first_top, first_rest, 0)
             else:
-                owned.append(apply_first(residual, diag_inv_local))
-        solved.append(owned)
-        held = [gather_rows(value) for value in owned]
-        gathered.append([assemble(pieces, order) for pieces in held])
-        if current + 1 < supernodes:
-            residuals = [
-                later[current * streams + i] - apply_pieces(sub_local, current, pieces)
-                for i, pieces in enumerate(held)
-            ]
+                whole = assemble(pieces, order)
+                if step % 2 == 0:
+                    owned = contract_last(whole, diag_inv_local[0, current])
+                elif current + 1 < supernodes:
+                    owned = later[current * streams + i] - contract_last(whole, sub_local[0, current])
+            if step % 2 == 0:
+                solved[current][i] = owned
+            else:
+                gathered[current][i] = whole
+            values[i] = owned
+            last = pieces
 
     by_stream = [[values[i] for values in gathered] for i in range(streams)]
     done = [tile_terms(values, tiles[0, 0], tile_source) for values in by_stream[:-1]]

time: 142 us -> 150 us (1.056)
  waiting for transfers between devices: 17.5 us -> 39.1 us
  Pallas kernels: 13.9 us -> 7.51 us
  matrix products: 13.7 us -> 7.53 us
    ppermute x57, waiting for transfers between devices: 12.4 us -> 34 us  [send(): return lax.ppermute(value, axis, pairs)]
    pallas_call x13, Pallas kernels: 13.9 us -> 7.51 us  [local_kernel(): pl.pallas_call(body, out_shape=list(outs), in_specs=specs or [VMEM] * len...]
    dot_general x48 -> x12, matrix products: 13.7 us -> 7.53 us  [contract_last(): lax.dot_general(left, right, (((left.ndim - 1,), (right.ndim - 1,)), ((),...]
  transfers between devices with their start and end apart: 61 -> 61, of which waited for: 12 -> 22; matrix products, arithmetic and copies ran while one was open for 11% -> 6% of each run, Pallas kernels for 7% -> 3%
where the time goes in v16:
time: 150 us; the launch traced here: 149 us
  starting transfers between devices  88.8 us (59%)
  waiting for transfers between devices  39.1 us (26%)
  matrix products  7.53 us (5%)
  Pallas kernels  7.51 us (5%)
  local copies, waits for them, and re-layouts  2.85 us (2%)
  between operations  2.17 us (1%)
    ppermute x57, starting transfers between devices, send(): return lax.ppermute(value, axis, pairs)  85.2 us
    ppermute x57, waiting for transfers between devices, send(): return lax.ppermute(value, axis, pairs)  34 us
    dot_general x12, matrix products, contract_last(): lax.dot_general(left, right, (((left.ndim - 1,), (right.ndim - 1,)), ((),...  7.53 us
    pallas_call x13, Pallas kernels, local_kernel(): pl.pallas_call(body, out_shape=list(outs), in_specs=specs or [VMEM] * len...  7.51 us
    ppermute x3, waiting for transfers between devices, swap(): return lax.ppermute(value, axis, pairs)  3.69 us
    ppermute x3, starting transfers between devices, swap(): return lax.ppermute(value, axis, pairs)  3.55 us
  transfers between devices with their start and end apart: 61, of which 22 were waited for; matrix products, arithmetic and copies ran while one was open for 6% of the time, Pallas kernels for 3%

profile of v16, /device:TPU:0, one launch (start us, length us, event | category | flops | bytes accessed | tf_op | source)
XLA Modules:
  0.0 149.3 jit_solution(7999670999389673206)
XLA Ops:
  0.6 1.0 copy-done.1
  1.9 3.1 %collective-permute-start = (f32[64,256]{1,0:T(8,128)S(1)}, f32[64,256]{1,0:T(8,128)S(1)}, u32[]{:S(2)}, u32[]{:S(2)}) collective-permute-start(f32[64,256]{1,0:T(8,128)S(1)} %get-tuple-element.37.refs_0_), channel_id=1, source_target_pairs={{0,1},{1,0},{2,3},{3,2},{4,5},{5,4},{6,7},{7,6},{8,9},{9,8},{10,11... | collective-permute-start | bytes 196616 | tf_op jit(solution)/shard_map/ppermute | solution.py:33
  5.0 2.6 %collective-permute-start.1 = (f32[64,256]{1,0:T(8,128)S(1)}, f32[64,256]{1,0:T(8,128)S(1)}, u32[]{:S(2)}, u32[]{:S(2)}) collective-permute-start(f32[64,256]{1,0:T(8,128)S(1)} %get-tuple-element.37.refs_0_), channel_id=1, source_target_pairs={{0,2},{1,3},{2,0},{3,1},{4,6},{5,7},{6,4},{7,5},{8,10},{9,11},{10,... | collective-permute-start | bytes 196616 | tf_op jit(solution)/shard_map/ppermute | solution.py:33
  7.6 1.9 %collective-permute-start.4 = (f32[64,256]{1,0:T(8,128)S(1)}, f32[64,256]{1,0:T(8,128)S(1)}, u32[]{:S(2)}, u32[]{:S(2)}) collective-permute-start(f32[64,256]{1,0:T(8,128)S(1)} %get-tuple-element.39.refs_0_), channel_id=1, source_target_pairs={{0,2},{1,3},{2,0},{3,1},{4,6},{5,7},{6,4},{7,5},{8,10},{9,11},{10,... | collective-permute-start | bytes 196616 | tf_op jit(solution)/shard_map/ppermute | solution.py:33
  9.5 1.9 %collective-permute-start.5 = (f32[64,256]{1,0:T(8,128)S(1)}, f32[64,256]{1,0:T(8,128)S(1)}, u32[]{:S(2)}, u32[]{:S(2)}) collective-permute-start(f32[64,256]{1,0:T(8,128)S(1)} %get-tuple-element.39.refs_0_), channel_id=1, source_target_pairs={{0,3},{1,2},{2,1},{3,0},{4,7},{5,6},{6,5},{7,4},{8,11},{9,10},{10,... | collective-permute-start | bytes 196616 | tf_op jit(solution)/shard_map/ppermute | solution.py:33
  11.4 1.4 fusion
  12.9 1.0 copy-done.2
  15.0 0.9 collective-permute-done.1.refs_2_
  16.3 3.4 %collective-permute-start.7 = (f32[64,256]{1,0:T(8,128)S(1)}, f32[64,256]{1,0:T(8,128)S(1)}, u32[]{:S(2)}, u32[]{:S(2)}) collective-permute-start(f32[64,256]{1,0:T(8,128)S(1)} %shard_map.114.refs_0_), channel_id=1, source_target_pairs={{0,2},{1,3},{2,0},{3,1},{4,6},{5,7},{6,4},{7,5},{8,10},{9,11},{10,... | collective-permute-start | bytes 196616 | tf_op jit(solution)/shard_map/ppermute | solution.py:33
  19.7 1.0 collective-permute-start.8
  20.8 4.2 %collective-permute-done.3.refs_1_ = f32[64,256]{1,0:T(8,128)S(1)} collective-permute-done((f32[64,256]{1,0:T(8,128)S(1)}, f32[64,256]{1,0:T(8,128)S(1)}, u32[]{:S(2)}, u32[]{:S(2)}) %collective-permute-start.3) | collective-permute-done | bytes 65568 | tf_op jit(solution)/shard_map/ppermute | solution.py:33
  25.4 2.6 %collective-permute-start.13 = (f32[64,256]{1,0:T(8,128)S(1)}, f32[64,256]{1,0:T(8,128)S(1)}, u32[]{:S(2)}, u32[]{:S(2)}) collective-permute-start(f32[64,256]{1,0:T(8,128)S(1)} %shard_map.115.refs_1_), channel_id=1, source_target_pairs={{0,2},{1,3},{2,0},{3,1},{4,6},{5,7},{6,4},{7,5},{8,10},{9,11},{10,... | collective-permute-start | bytes 196616 | tf_op jit(solution)/shard_map/ppermute | solution.py:33
  29.0 4.1 %collective-permute-done.6 = f32[64,256]{1,0:T(8,128)S(1)} collective-permute-done((f32[64,256]{1,0:T(8,128)S(1)}, f32[64,256]{1,0:T(8,128)S(1)}, u32[]{:S(2)}, u32[]{:S(2)}) %collective-permute-start.6) | collective-permute-done | bytes 65568 | tf_op jit(solution)/shard_map/ppermute | solution.py:33
  33.1 1.2 collective-permute-start.9
  35.1 3.1 %collective-permute-start.11 = (f32[64,256]{1,0:T(8,128)S(1)}, f32[64,256]{1,0:T(8,128)S(1)}, u32[]{:S(2)}, u32[]{:S(2)}) collective-permute-start(f32[64,256]{1,0:T(8,128)S(1)} %get-tuple-element.42), channel_id=1, source_target_pairs={{0,2},{1,3},{2,0},{3,1},{4,6},{5,7},{6,4},{7,5},{8,10},{9,11},{10,... | collective-permute-start | bytes 196616 | tf_op jit(solution)/shard_map/ppermute | solution.py:33
  39.0 0.6 constant_dynamic-update-slice_fusion.43
  39.6 3.8 %collective-permute-start.16 = (f32[64,256]{1,0:T(8,128)S(1)}, f32[64,256]{1,0:T(8,128)S(1)}, u32[]{:S(2)}, u32[]{:S(2)}) collective-permute-start(f32[64,256]{1,0:T(8,128)S(1)} %get-tuple-element.43), channel_id=1, source_target_pairs={{0,2},{1,3},{2,0},{3,1},{4,6},{5,7},{6,4},{7,5},{8,10},{9,11},{10,... | collective-permute-start | bytes 196616 | tf_op jit(solution)/shard_map/ppermute | solution.py:33
  43.4 0.6 collective-permute-start.17
  45.7 3.0 %collective-permute-start.19 = (f32[64,256]{1,0:T(8,128)S(1)}, f32[64,256]{1,0:T(8,128)S(1)}, u32[]{:S(2)}, u32[]{:S(2)}) collective-permute-start(f32[64,256]{1,0:T(8,128)S(1)} %get-tuple-element.44.refs_2_), channel_id=1, source_target_pairs={{0,2},{1,3},{2,0},{3,1},{4,6},{5,7},{6,4},{7,5},{8,10},{9,11},{10,... | collective-permute-start | bytes 196616 | tf_op jit(solution)/shard_map/ppermute | solution.py:33
  48.6 1.0 collective-permute-start.20
  50.9 3.7 %collective-permute-start.25 = (f32[64,256]{1,0:T(8,128)S(1)}, f32[64,256]{1,0:T(8,128)S(1)}, u32[]{:S(2)}, u32[]{:S(2)}) collective-permute-start(f32[64,256]{1,0:T(8,128)S(1)} %get-tuple-element.45.refs_3_), channel_id=1, source_target_pairs={{0,2},{1,3},{2,0},{3,1},{4,6},{5,7},{6,4},{7,5},{8,10},{9,11},{10,... | collective-permute-start | bytes 196616 | tf_op jit(solution)/shard_map/ppermute | solution.py:33
  55.4 0.6 constant_dynamic-update-slice_fusion.35
  56.1 5.4 %collective-permute-start.23 = (f32[64,256]{1,0:T(8,128)S(1)}, f32[64,256]{1,0:T(8,128)S(1)}, u32[]{:S(2)}, u32[]{:S(2)}) collective-permute-start(f32[64,256]{1,0:T(8,128)S(1)} %get-tuple-element.46), channel_id=1, source_target_pairs={{0,2},{1,3},{2,0},{3,1},{4,6},{5,7},{6,4},{7,5},{8,10},{9,11},{10,... | collective-permute-start | bytes 196616 | tf_op jit(solution)/shard_map/ppermute | solution.py:33
  61.5 0.6 collective-permute-start.22
  62.2 0.6 constant_dynamic-update-slice_fusion.27
  62.9 3.8 %collective-permute-start.28 = (f32[64,256]{1,0:T(8,128)S(1)}, f32[64,256]{1,0:T(8,128)S(1)}, u32[]{:S(2)}, u32[]{:S(2)}) collective-permute-start(f32[64,256]{1,0:T(8,128)S(1)} %get-tuple-element.47), channel_id=1, source_target_pairs={{0,2},{1,3},{2,0},{3,1},{4,6},{5,7},{6,4},{7,5},{8,10},{9,11},{10,... | collective-permute-start | bytes 196616 | tf_op jit(solution)/shard_map/ppermute | solution.py:33
  66.7 2.1 %collective-permute-done.22 = f32[64,256]{1,0:T(8,128)S(1)} collective-permute-done((f32[64,256]{1,0:T(8,128)S(1)}, f32[64,256]{1,0:T(8,128)S(1)}, u32[]{:S(2)}, u32[]{:S(2)}) %collective-permute-start.22) | collective-permute-done | bytes 65568 | tf_op jit(solution)/shard_map/ppermute | solution.py:33
  69.5 2.8 %collective-permute-start.31 = (f32[64,256]{1,0:T(8,128)S(1)}, f32[64,256]{1,0:T(8,128)S(1)}, u32[]{:S(2)}, u32[]{:S(2)}) collective-permute-start(f32[64,256]{1,0:T(8,128)S(1)} %get-tuple-element.48.refs_4_), channel_id=1, source_target_pairs={{0,2},{1,3},{2,0},{3,1},{4,6},{5,7},{6,4},{7,5},{8,10},{9,11},{10,... | collective-permute-start | bytes 196616 | tf_op jit(solution)/shard_map/ppermute | solution.py:33
  72.3 1.6 %collective-permute-start.32 = (f32[64,256]{1,0:T(8,128)S(1)}, f32[64,256]{1,0:T(8,128)S(1)}, u32[]{:S(2)}, u32[]{:S(2)}) collective-permute-start(f32[64,256]{1,0:T(8,128)S(1)} %get-tuple-element.48.refs_4_), channel_id=1, source_target_pairs={{0,3},{1,2},{2,1},{3,0},{4,7},{5,6},{6,5},{7,4},{8,11},{9,10},{10,... | collective-permute-start | bytes 196616 | tf_op jit(solution)/shard_map/ppermute | solution.py:33
  74.0 0.7 collective-permute-done.27
  75.4 2.6 %collective-permute-start.37 = (f32[64,256]{1,0:T(8,128)S(1)}, f32[64,256]{1,0:T(8,128)S(1)}, u32[]{:S(2)}, u32[]{:S(2)}) collective-permute-start(f32[64,256]{1,0:T(8,128)S(1)} %get-tuple-element.49.refs_5_), channel_id=1, source_target_pairs={{0,2},{1,3},{2,0},{3,1},{4,6},{5,7},{6,4},{7,5},{8,10},{9,11},{10,... | collective-permute-start | bytes 196616 | tf_op jit(solution)/shard_map/ppermute | solution.py:33
  78.0 1.8 %collective-permute-start.38 = (f32[64,256]{1,0:T(8,128)S(1)}, f32[64,256]{1,0:T(8,128)S(1)}, u32[]{:S(2)}, u32[]{:S(2)}) collective-permute-start(f32[64,256]{1,0:T(8,128)S(1)} %get-tuple-element.49.refs_5_), channel_id=1, source_target_pairs={{0,3},{1,2},{2,1},{3,0},{4,7},{5,6},{6,5},{7,4},{8,11},{9,10},{10,... | collective-permute-start | bytes 196616 | tf_op jit(solution)/shard_map/ppermute | solution.py:33
  80.9 2.7 %collective-permute-start.35 = (f32[64,256]{1,0:T(8,128)S(1)}, f32[64,256]{1,0:T(8,128)S(1)}, u32[]{:S(2)}, u32[]{:S(2)}) collective-permute-start(f32[64,256]{1,0:T(8,128)S(1)} %get-tuple-element.50), channel_id=1, source_target_pairs={{0,2},{1,3},{2,0},{3,1},{4,6},{5,7},{6,4},{7,5},{8,10},{9,11},{10,... | collective-permute-start | bytes 196616 | tf_op jit(solution)/shard_map/ppermute | solution.py:33
  83.6 1.7 %collective-permute-start.36 = (f32[64,256]{1,0:T(8,128)S(1)}, f32[64,256]{1,0:T(8,128)S(1)}, u32[]{:S(2)}, u32[]{:S(2)}) collective-permute-start(f32[64,256]{1,0:T(8,128)S(1)} %get-tuple-element.50), channel_id=1, source_target_pairs={{0,3},{1,2},{2,1},{3,0},{4,7},{5,6},{6,5},{7,4},{8,11},{9,10},{10,... | collective-permute-start | bytes 196616 | tf_op jit(solution)/shard_map/ppermute | solution.py:33
  85.9 0.6 constant_dynamic-update-slice_fusion.11
  86.5 2.7 %collective-permute-start.40 = (f32[64,256]{1,0:T(8,128)S(1)}, f32[64,256]{1,0:T(8,128)S(1)}, u32[]{:S(2)}, u32[]{:S(2)}) collective-permute-start(f32[64,256]{1,0:T(8,128)S(1)} %get-tuple-element.51), channel_id=1, source_target_pairs={{0,2},{1,3},{2,0},{3,1},{4,6},{5,7},{6,4},{7,5},{8,10},{9,11},{10,... | collective-permute-start | bytes 196616 | tf_op jit(solution)/shard_map/ppermute | solution.py:33
  89.2 1.8 %collective-permute-start.41 = (f32[64,256]{1,0:T(8,128)S(1)}, f32[64,256]{1,0:T(8,128)S(1)}, u32[]{:S(2)}, u32[]{:S(2)}) collective-permute-start(f32[64,256]{1,0:T(8,128)S(1)} %get-tuple-element.51), channel_id=1, source_target_pairs={{0,3},{1,2},{2,1},{3,0},{4,7},{5,6},{6,5},{7,4},{8,11},{9,10},{10,... | collective-permute-start | bytes 196616 | tf_op jit(solution)/shard_map/ppermute | solution.py:33
  91.0 5.2 %collective-permute-done.39 = f32[64,256]{1,0:T(8,128)S(1)} collective-permute-done((f32[64,256]{1,0:T(8,128)S(1)}, f32[64,256]{1,0:T(8,128)S(1)}, u32[]{:S(2)}, u32[]{:S(2)}) %collective-permute-start.39) | collective-permute-done | bytes 65568 | tf_op jit(solution)/shard_map/ppermute | solution.py:33
  96.9 2.3 %collective-permute-start.43 = (f32[64,256]{1,0:T(8,128)S(1)}, f32[64,256]{1,0:T(8,128)S(1)}, u32[]{:S(2)}, u32[]{:S(2)}) collective-permute-start(f32[64,256]{1,0:T(8,128)S(1)} %get-tuple-element.52.refs_6_), channel_id=1, source_target_pairs={{0,2},{1,3},{2,0},{3,1},{4,6},{5,7},{6,4},{7,5},{8,10},{9,11},{10,... | collective-permute-start | bytes 196616 | tf_op jit(solution)/shard_map/ppermute | solution.py:33
  99.3 1.9 %collective-permute-start.44 = (f32[64,256]{1,0:T(8,128)S(1)}, f32[64,256]{1,0:T(8,128)S(1)}, u32[]{:S(2)}, u32[]{:S(2)}) collective-permute-start(f32[64,256]{1,0:T(8,128)S(1)} %get-tuple-element.52.refs_6_), channel_id=1, source_target_pairs={{0,3},{1,2},{2,1},{3,0},{4,7},{5,6},{6,5},{7,4},{8,11},{9,10},{10,... | collective-permute-start | bytes 196616 | tf_op jit(solution)/shard_map/ppermute | solution.py:33
  101.8 2.5 %collective-permute-start.46 = (f32[64,256]{1,0:T(8,128)S(1)}, f32[64,256]{1,0:T(8,128)S(1)}, u32[]{:S(2)}, u32[]{:S(2)}) collective-permute-start(f32[64,256]{1,0:T(8,128)S(1)} %get-tuple-element.53.refs_7_), channel_id=1, source_target_pairs={{0,2},{1,3},{2,0},{3,1},{4,6},{5,7},{6,4},{7,5},{8,10},{9,11},{10,... | collective-permute-start | bytes 196616 | tf_op jit(solution)/shard_map/ppermute | solution.py:33
  104.4 1.9 %collective-permute-start.47 = (f32[64,256]{1,0:T(8,128)S(1)}, f32[64,256]{1,0:T(8,128)S(1)}, u32[]{:S(2)}, u32[]{:S(2)}) collective-permute-start(f32[64,256]{1,0:T(8,128)S(1)} %get-tuple-element.53.refs_7_), channel_id=1, source_target_pairs={{0,3},{1,2},{2,1},{3,0},{4,7},{5,6},{6,5},{7,4},{8,11},{9,10},{10,... | collective-permute-start | bytes 196616 | tf_op jit(solution)/shard_map/ppermute | solution.py:33
  106.4 1.2 shard_map.117.refs_0_
  107.6 3.5 %collective-permute-done.45 = f32[64,256]{1,0:T(8,128)S(1)} collective-permute-done((f32[64,256]{1,0:T(8,128)S(1)}, f32[64,256]{1,0:T(8,128)S(1)}, u32[]{:S(2)}, u32[]{:S(2)}) %collective-permute-start.45) | collective-permute-done | bytes 65568 | tf_op jit(solution)/shard_map/ppermute | solution.py:33
  111.2 1.2 shard_map.118
  112.5 1.3 collective-permute-done.48.refs_1_
  113.9 1.6 %collective-permute-start.49 = (f32[2,16,512]{2,1,0:T(8,128)S(1)}, f32[2,16,512]{2,1,0:T(8,128)S(1)}, u32[]{:S(2)}, u32[]{:S(2)}) collective-permute-start(f32[2,16,512]{2,1,0:T(8,128)S(1)} %get-tuple-element.58), channel_id=1, source_target_pairs={{0,8},{4,12},{8,0},{12,4},{16,24},{20,28},{24,16},{28,20},{1,9},{5... | collective-permute-start | bytes 196616 | tf_op jit(solution)/shard_map/ppermute | solution.py:74
  115.4 1.5 %collective-permute-start.50 = (f32[2,16,512]{2,1,0:T(8,128)S(1)}, f32[2,16,512]{2,1,0:T(8,128)S(1)}, u32[]{:S(2)}, u32[]{:S(2)}) collective-permute-start(f32[2,16,512]{2,1,0:T(8,128)S(1)} %get-tuple-element.59), channel_id=1, source_target_pairs={{0,16},{4,20},{8,24},{12,28},{16,0},{20,4},{24,8},{28,12},{1,17},{... | collective-permute-start | bytes 196616 | tf_op jit(solution)/shard_map/ppermute | solution.py:74
  117.4 1.0 shard_map.119
  118.4 1.3 collective-permute-done.50.refs_2_
  119.7 2.4 %collective-permute-done.51.refs_3_ = f32[2,16,512]{2,1,0:T(8,128)S(1)} collective-permute-done((f32[2,16,512]{2,1,0:T(8,128)S(1)}, f32[2,16,512]{2,1,0:T(8,128)S(1)}, u32[]{:S(2)}, u32[]{:S(2)}) %collective-permute-start.51) | collective-permute-done | bytes 65568 | tf_op jit(solution)/shard_map/ppermute | solution.py:74
  122.7 2.4 %collective-permute-start.53 = (f32[16,1280]{1,0:T(8,128)S(1)}, f32[16,1280]{1,0:T(8,128)S(1)}, u32[]{:S(2)}, u32[]{:S(2)}) collective-permute-start(f32[16,1280]{1,0:T(8,128)S(1)} %get-tuple-element.64), channel_id=1, source_target_pairs={{0,2},{1,3},{2,0},{3,1},{4,6},{5,7},{6,4},{7,5},{8,10},{9,11},{10,... | collective-permute-start | bytes 245768 | tf_op jit(solution)/shard_map/ppermute | solution.py:33
  125.1 1.9 %collective-permute-start.54 = (f32[16,1280]{1,0:T(8,128)S(1)}, f32[16,1280]{1,0:T(8,128)S(1)}, u32[]{:S(2)}, u32[]{:S(2)}) collective-permute-start(f32[16,1280]{1,0:T(8,128)S(1)} %get-tuple-element.65), channel_id=1, source_target_pairs={{0,3},{1,2},{2,1},{3,0},{4,7},{5,6},{6,5},{7,4},{8,11},{9,10},{10,... | collective-permute-start | bytes 245768 | tf_op jit(solution)/shard_map/ppermute | solution.py:33
  127.4 2.4 %collective-permute-done.53.refs_2_ = f32[16,1280]{1,0:T(8,128)S(1)} collective-permute-done((f32[16,1280]{1,0:T(8,128)S(1)}, f32[16,1280]{1,0:T(8,128)S(1)}, u32[]{:S(2)}, u32[]{:S(2)}) %collective-permute-start.53) | collective-permute-done | bytes 81952 | tf_op jit(solution)/shard_map/ppermute | solution.py:33
  129.9 1.6 %collective-permute-done.54.refs_3_ = f32[16,1280]{1,0:T(8,128)S(1)} collective-permute-done((f32[16,1280]{1,0:T(8,128)S(1)}, f32[16,1280]{1,0:T(8,128)S(1)}, u32[]{:S(2)}, u32[]{:S(2)}) %collective-permute-start.54) | collective-permute-done | bytes 81952 | tf_op jit(solution)/shard_map/ppermute | solution.py:33
  131.8 0.8 collective-permute-start.55
  132.6 1.7 %collective-permute-start.56 = (f32[16,256]{1,0:T(8,128)S(1)}, f32[16,256]{1,0:T(8,128)S(1)}, u32[]{:S(2)}, u32[]{:S(2)}) collective-permute-start(f32[16,256]{1,0:T(8,128)S(1)} %get-tuple-element.68.refs_0_.refs_6_), channel_id=1, source_target_pairs={{0,2},{1,3},{2,0},{3,1},{4,6},{5,7},{6,4},{7,5},{8,10},{9,11},{10,... | collective-permute-start | bytes 49160 | tf_op jit(solution)/shard_map/ppermute | solution.py:33
  134.3 1.9 %collective-permute-start.57 = (f32[16,256]{1,0:T(8,128)S(1)}, f32[16,256]{1,0:T(8,128)S(1)}, u32[]{:S(2)}, u32[]{:S(2)}) collective-permute-start(f32[16,256]{1,0:T(8,128)S(1)} %get-tuple-element.68.refs_0_.refs_6_), channel_id=1, source_target_pairs={{0,3},{1,2},{2,1},{3,0},{4,7},{5,6},{6,5},{7,4},{8,11},{9,10},{10,... | collective-permute-start | bytes 49160 | tf_op jit(solution)/shard_map/ppermute | solution.py:33
  136.2 1.0 collective-permute-done.56.refs_2_
  137.2 2.7 %collective-permute-done.57.refs_3_ = f32[16,256]{1,0:T(8,128)S(1)} collective-permute-done((f32[16,256]{1,0:T(8,128)S(1)}, f32[16,256]{1,0:T(8,128)S(1)}, u32[]{:S(2)}, u32[]{:S(2)}) %collective-permute-start.57) | collective-permute-done | bytes 16416 | tf_op jit(solution)/shard_map/ppermute | solution.py:33
  140.3 2.5 %collective-permute-start.59 = (f32[16,256]{1,0:T(8,128)S(1)}, f32[16,256]{1,0:T(8,128)S(1)}, u32[]{:S(2)}, u32[]{:S(2)}) collective-permute-start(f32[16,256]{1,0:T(8,128)S(1)} %shard_map.124.refs_0_), channel_id=1, source_target_pairs={{0,2},{1,3},{2,0},{3,1},{4,6},{5,7},{6,4},{7,5},{8,10},{9,11},{10,... | collective-permute-start | bytes 49160 | tf_op jit(solution)/shard_map/ppermute | solution.py:33
  142.8 1.9 %collective-permute-start.60 = (f32[16,256]{1,0:T(8,128)S(1)}, f32[16,256]{1,0:T(8,128)S(1)}, u32[]{:S(2)}, u32[]{:S(2)}) collective-permute-start(f32[16,256]{1,0:T(8,128)S(1)} %shard_map.124.refs_0_), channel_id=1, source_target_pairs={{0,3},{1,2},{2,1},{3,0},{4,7},{5,6},{6,5},{7,4},{8,11},{9,10},{10,... | collective-permute-start | bytes 49160 | tf_op jit(solution)/shard_map/ppermute | solution.py:33
  145.0 3.3 %collective-permute-done.60.refs_3_ = f32[16,256]{1,0:T(8,128)S(1)} collective-permute-done((f32[16,256]{1,0:T(8,128)S(1)}, f32[16,256]{1,0:T(8,128)S(1)}, u32[]{:S(2)}, u32[]{:S(2)}) %collective-permute-start.60) | collective-permute-done | bytes 16416 | tf_op jit(solution)/shard_map/ppermute | solution.py:33
  148.3 1.0 shard_map.125
  (161 shorter events, 14.6 us)
Async XLA Ops:
  1.9 13.0 %collective-permute-start = (f32[64,256]{1,0:T(8,128)S(1)}, f32[64,256]{1,0:T(8,128)S(1)}, u32[]{:S(2)}, u32[]{:S(2)}) collective-permute-start(f32[64,256]{1,0:T(8,128)S(1)} %get-tuple-element.37.refs_0_), channel_id=1, source_target_pairs={{0,1},{1,0},{2,3},{3,2},{4,5},{5,4},{6,7},{7,6},{8,9},{9,8},{10,11... | collective-permute-start | bytes 196616 | tf_op jit(solution)/shard_map/ppermute | solution.py:33
  5.0 10.9 %collective-permute-start.1 = (f32[64,256]{1,0:T(8,128)S(1)}, f32[64,256]{1,0:T(8,128)S(1)}, u32[]{:S(2)}, u32[]{:S(2)}) collective-permute-start(f32[64,256]{1,0:T(8,128)S(1)} %get-tuple-element.37.refs_0_), channel_id=1, source_target_pairs={{0,2},{1,3},{2,0},{3,1},{4,6},{5,7},{6,4},{7,5},{8,10},{9,11},{10,... | collective-permute-start | bytes 196616 | tf_op jit(solution)/shard_map/ppermute | solution.py:33
  7.6 8.3 %collective-permute-start.2 = (f32[64,256]{1,0:T(8,128)S(1)}, f32[64,256]{1,0:T(8,128)S(1)}, u32[]{:S(2)}, u32[]{:S(2)}) collective-permute-start(f32[64,256]{1,0:T(8,128)S(1)} %get-tuple-element.37.refs_0_), channel_id=1, source_target_pairs={{0,3},{1,2},{2,1},{3,0},{4,7},{5,6},{6,5},{7,4},{8,11},{9,10},{10,... | collective-permute-start | bytes 196616 | tf_op jit(solution)/shard_map/ppermute | solution.py:33
  7.6 13.2 %collective-permute-start.4 = (f32[64,256]{1,0:T(8,128)S(1)}, f32[64,256]{1,0:T(8,128)S(1)}, u32[]{:S(2)}, u32[]{:S(2)}) collective-permute-start(f32[64,256]{1,0:T(8,128)S(1)} %get-tuple-element.39.refs_0_), channel_id=1, source_target_pairs={{0,2},{1,3},{2,0},{3,1},{4,6},{5,7},{6,4},{7,5},{8,10},{9,11},{10,... | collective-permute-start | bytes 196616 | tf_op jit(solution)/shard_map/ppermute | solution.py:33
  9.5 11.3 %collective-permute-start.5 = (f32[64,256]{1,0:T(8,128)S(1)}, f32[64,256]{1,0:T(8,128)S(1)}, u32[]{:S(2)}, u32[]{:S(2)}) collective-permute-start(f32[64,256]{1,0:T(8,128)S(1)} %get-tuple-element.39.refs_0_), channel_id=1, source_target_pairs={{0,3},{1,2},{2,1},{3,0},{4,7},{5,6},{6,5},{7,4},{8,11},{9,10},{10,... | collective-permute-start | bytes 196616 | tf_op jit(solution)/shard_map/ppermute | solution.py:33
  16.3 18.0 %collective-permute-start.7 = (f32[64,256]{1,0:T(8,128)S(1)}, f32[64,256]{1,0:T(8,128)S(1)}, u32[]{:S(2)}, u32[]{:S(2)}) collective-permute-start(f32[64,256]{1,0:T(8,128)S(1)} %shard_map.114.refs_0_), channel_id=1, source_target_pairs={{0,2},{1,3},{2,0},{3,1},{4,6},{5,7},{6,4},{7,5},{8,10},{9,11},{10,... | collective-permute-start | bytes 196616 | tf_op jit(solution)/shard_map/ppermute | solution.py:33
  19.7 14.7 %collective-permute-start.8 = (f32[64,256]{1,0:T(8,128)S(1)}, f32[64,256]{1,0:T(8,128)S(1)}, u32[]{:S(2)}, u32[]{:S(2)}) collective-permute-start(f32[64,256]{1,0:T(8,128)S(1)} %shard_map.114.refs_0_), channel_id=1, source_target_pairs={{0,3},{1,2},{2,1},{3,0},{4,7},{5,6},{6,5},{7,4},{8,11},{9,10},{10,... | collective-permute-start | bytes 196616 | tf_op jit(solution)/shard_map/ppermute | solution.py:33
  20.7 4.3 %collective-permute-start.3 = (f32[64,256]{1,0:T(8,128)S(1)}, f32[64,256]{1,0:T(8,128)S(1)}, u32[]{:S(2)}, u32[]{:S(2)}) collective-permute-start(f32[64,256]{1,0:T(8,128)S(1)} %get-tuple-element.39.refs_0_), channel_id=1, source_target_pairs={{0,1},{1,0},{2,3},{3,2},{4,5},{5,4},{6,7},{7,6},{8,9},{9,8},{10,11... | collective-permute-start | bytes 196616 | tf_op jit(solution)/shard_map/ppermute | solution.py:33
  20.8 24.2 %copy-start.8 = (f32[1,4,256,1024]{3,2,1,0:T(8,128)S(1)}, f32[1,4,256,1024]{3,2,1,0:T(8,128)}, u32[]{:S(2)}) copy-start(f32[1,4,256,1024]{3,2,1,0:T(8,128)} %param.11) | copy-start | bytes 12582916
  25.4 13.5 %collective-permute-start.13 = (f32[64,256]{1,0:T(8,128)S(1)}, f32[64,256]{1,0:T(8,128)S(1)}, u32[]{:S(2)}, u32[]{:S(2)}) collective-permute-start(f32[64,256]{1,0:T(8,128)S(1)} %shard_map.115.refs_1_), channel_id=1, source_target_pairs={{0,2},{1,3},{2,0},{3,1},{4,6},{5,7},{6,4},{7,5},{8,10},{9,11},{10,... | collective-permute-start | bytes 196616 | tf_op jit(solution)/shard_map/ppermute | solution.py:33
  28.0 10.9 %collective-permute-start.14 = (f32[64,256]{1,0:T(8,128)S(1)}, f32[64,256]{1,0:T(8,128)S(1)}, u32[]{:S(2)}, u32[]{:S(2)}) collective-permute-start(f32[64,256]{1,0:T(8,128)S(1)} %shard_map.115.refs_1_), channel_id=1, source_target_pairs={{0,3},{1,2},{2,1},{3,0},{4,7},{5,6},{6,5},{7,4},{8,11},{9,10},{10,... | collective-permute-start | bytes 196616 | tf_op jit(solution)/shard_map/ppermute | solution.py:33
  28.6 4.6 %collective-permute-start.6 = (f32[64,256]{1,0:T(8,128)S(1)}, f32[64,256]{1,0:T(8,128)S(1)}, u32[]{:S(2)}, u32[]{:S(2)}) collective-permute-start(f32[64,256]{1,0:T(8,128)S(1)} %shard_map.114.refs_0_), channel_id=1, source_target_pairs={{0,1},{1,0},{2,3},{3,2},{4,5},{5,4},{6,7},{7,6},{8,9},{9,8},{10,11... | collective-permute-start | bytes 196616 | tf_op jit(solution)/shard_map/ppermute | solution.py:33
  33.1 5.8 %collective-permute-start.9 = (f32[64,256]{1,0:T(8,128)S(1)}, f32[64,256]{1,0:T(8,128)S(1)}, u32[]{:S(2)}, u32[]{:S(2)}) collective-permute-start(f32[64,256]{1,0:T(8,128)S(1)} %shard_map.115.refs_1_), channel_id=1, source_target_pairs={{0,1},{1,0},{2,3},{3,2},{4,5},{5,4},{6,7},{7,6},{8,9},{9,8},{10,11... | collective-permute-start | bytes 196616 | tf_op jit(solution)/shard_map/ppermute | solution.py:33
  35.1 9.7 %collective-permute-start.11 = (f32[64,256]{1,0:T(8,128)S(1)}, f32[64,256]{1,0:T(8,128)S(1)}, u32[]{:S(2)}, u32[]{:S(2)}) collective-permute-start(f32[64,256]{1,0:T(8,128)S(1)} %get-tuple-element.42), channel_id=1, source_target_pairs={{0,2},{1,3},{2,0},{3,1},{4,6},{5,7},{6,4},{7,5},{8,10},{9,11},{10,... | collective-permute-start | bytes 196616 | tf_op jit(solution)/shard_map/ppermute | solution.py:33
  38.3 6.7 %collective-permute-start.12 = (f32[64,256]{1,0:T(8,128)S(1)}, f32[64,256]{1,0:T(8,128)S(1)}, u32[]{:S(2)}, u32[]{:S(2)}) collective-permute-start(f32[64,256]{1,0:T(8,128)S(1)} %get-tuple-element.42), channel_id=1, source_target_pairs={{0,3},{1,2},{2,1},{3,0},{4,7},{5,6},{6,5},{7,4},{8,11},{9,10},{10,... | collective-permute-start | bytes 196616 | tf_op jit(solution)/shard_map/ppermute | solution.py:33
  38.9 5.6 %collective-permute-start.10 = (f32[64,256]{1,0:T(8,128)S(1)}, f32[64,256]{1,0:T(8,128)S(1)}, u32[]{:S(2)}, u32[]{:S(2)}) collective-permute-start(f32[64,256]{1,0:T(8,128)S(1)} %get-tuple-element.42), channel_id=1, source_target_pairs={{0,1},{1,0},{2,3},{3,2},{4,5},{5,4},{6,7},{7,6},{8,9},{9,8},{10,11... | collective-permute-start | bytes 196616 | tf_op jit(solution)/shard_map/ppermute | solution.py:33
  39.6 10.5 %collective-permute-start.16 = (f32[64,256]{1,0:T(8,128)S(1)}, f32[64,256]{1,0:T(8,128)S(1)}, u32[]{:S(2)}, u32[]{:S(2)}) collective-permute-start(f32[64,256]{1,0:T(8,128)S(1)} %get-tuple-element.43), channel_id=1, source_target_pairs={{0,2},{1,3},{2,0},{3,1},{4,6},{5,7},{6,4},{7,5},{8,10},{9,11},{10,... | collective-permute-start | bytes 196616 | tf_op jit(solution)/shard_map/ppermute | solution.py:33
  43.4 6.7 %collective-permute-start.17 = (f32[64,256]{1,0:T(8,128)S(1)}, f32[64,256]{1,0:T(8,128)S(1)}, u32[]{:S(2)}, u32[]{:S(2)}) collective-permute-start(f32[64,256]{1,0:T(8,128)S(1)} %get-tuple-element.43), channel_id=1, source_target_pairs={{0,3},{1,2},{2,1},{3,0},{4,7},{5,6},{6,5},{7,4},{8,11},{9,10},{10,... | collective-permute-start | bytes 196616 | tf_op jit(solution)/shard_map/ppermute | solution.py:33
  44.5 5.3 %collective-permute-start.15 = (f32[64,256]{1,0:T(8,128)S(1)}, f32[64,256]{1,0:T(8,128)S(1)}, u32[]{:S(2)}, u32[]{:S(2)}) collective-permute-start(f32[64,256]{1,0:T(8,128)S(1)} %get-tuple-element.43), channel_id=1, source_target_pairs={{0,1},{1,0},{2,3},{3,2},{4,5},{5,4},{6,7},{7,6},{8,9},{9,8},{10,11... | collective-permute-start | bytes 196616 | tf_op jit(solution)/shard_map/ppermute | solution.py:33
  45.7 9.7 %collective-permute-start.19 = (f32[64,256]{1,0:T(8,128)S(1)}, f32[64,256]{1,0:T(8,128)S(1)}, u32[]{:S(2)}, u32[]{:S(2)}) collective-permute-start(f32[64,256]{1,0:T(8,128)S(1)} %get-tuple-element.44.refs_2_), channel_id=1, source_target_pairs={{0,2},{1,3},{2,0},{3,1},{4,6},{5,7},{6,4},{7,5},{8,10},{9,11},{10,... | collective-permute-start | bytes 196616 | tf_op jit(solution)/shard_map/ppermute | solution.py:33
  48.6 6.8 %collective-permute-start.20 = (f32[64,256]{1,0:T(8,128)S(1)}, f32[64,256]{1,0:T(8,128)S(1)}, u32[]{:S(2)}, u32[]{:S(2)}) collective-permute-start(f32[64,256]{1,0:T(8,128)S(1)} %get-tuple-element.44.refs_2_), channel_id=1, source_target_pairs={{0,3},{1,2},{2,1},{3,0},{4,7},{5,6},{6,5},{7,4},{8,11},{9,10},{10,... | collective-permute-start | bytes 196616 | tf_op jit(solution)/shard_map/ppermute | solution.py:33
  49.8 5.2 %collective-permute-start.18 = (f32[64,256]{1,0:T(8,128)S(1)}, f32[64,256]{1,0:T(8,128)S(1)}, u32[]{:S(2)}, u32[]{:S(2)}) collective-permute-start(f32[64,256]{1,0:T(8,128)S(1)} %get-tuple-element.44.refs_2_), channel_id=1, source_target_pairs={{0,1},{1,0},{2,3},{3,2},{4,5},{5,4},{6,7},{7,6},{8,9},{9,8},{10,11... | collective-permute-start | bytes 196616 | tf_op jit(solution)/shard_map/ppermute | solution.py:33
  50.9 11.3 %collective-permute-start.25 = (f32[64,256]{1,0:T(8,128)S(1)}, f32[64,256]{1,0:T(8,128)S(1)}, u32[]{:S(2)}, u32[]{:S(2)}) collective-permute-start(f32[64,256]{1,0:T(8,128)S(1)} %get-tuple-element.45.refs_3_), channel_id=1, source_target_pairs={{0,2},{1,3},{2,0},{3,1},{4,6},{5,7},{6,4},{7,5},{8,10},{9,11},{10,... | collective-permute-start | bytes 196616 | tf_op jit(solution)/shard_map/ppermute | solution.py:33
  54.6 7.6 %collective-permute-start.26 = (f32[64,256]{1,0:T(8,128)S(1)}, f32[64,256]{1,0:T(8,128)S(1)}, u32[]{:S(2)}, u32[]{:S(2)}) collective-permute-start(f32[64,256]{1,0:T(8,128)S(1)} %get-tuple-element.45.refs_3_), channel_id=1, source_target_pairs={{0,3},{1,2},{2,1},{3,0},{4,7},{5,6},{6,5},{7,4},{8,11},{9,10},{10,... | collective-permute-start | bytes 196616 | tf_op jit(solution)/shard_map/ppermute | solution.py:33
  55.0 6.5 %collective-permute-start.21 = (f32[64,256]{1,0:T(8,128)S(1)}, f32[64,256]{1,0:T(8,128)S(1)}, u32[]{:S(2)}, u32[]{:S(2)}) collective-permute-start(f32[64,256]{1,0:T(8,128)S(1)} %get-tuple-element.45.refs_3_), channel_id=1, source_target_pairs={{0,1},{1,0},{2,3},{3,2},{4,5},{5,4},{6,7},{7,6},{8,9},{9,8},{10,11... | collective-permute-start | bytes 196616 | tf_op jit(solution)/shard_map/ppermute | solution.py:33
  56.1 12.8 %collective-permute-start.23 = (f32[64,256]{1,0:T(8,128)S(1)}, f32[64,256]{1,0:T(8,128)S(1)}, u32[]{:S(2)}, u32[]{:S(2)}) collective-permute-start(f32[64,256]{1,0:T(8,128)S(1)} %get-tuple-element.46), channel_id=1, source_target_pairs={{0,2},{1,3},{2,0},{3,1},{4,6},{5,7},{6,4},{7,5},{8,10},{9,11},{10,... | collective-permute-start | bytes 196616 | tf_op jit(solution)/shard_map/ppermute | solution.py:33
  61.5 7.4 %collective-permute-start.24 = (f32[64,256]{1,0:T(8,128)S(1)}, f32[64,256]{1,0:T(8,128)S(1)}, u32[]{:S(2)}, u32[]{:S(2)}) collective-permute-start(f32[64,256]{1,0:T(8,128)S(1)} %get-tuple-element.46), channel_id=1, source_target_pairs={{0,3},{1,2},{2,1},{3,0},{4,7},{5,6},{6,5},{7,4},{8,11},{9,10},{10,... | collective-permute-start | bytes 196616 | tf_op jit(solution)/shard_map/ppermute | solution.py:33
  61.5 7.3 %collective-permute-start.22 = (f32[64,256]{1,0:T(8,128)S(1)}, f32[64,256]{1,0:T(8,128)S(1)}, u32[]{:S(2)}, u32[]{:S(2)}) collective-permute-start(f32[64,256]{1,0:T(8,128)S(1)} %get-tuple-element.46), channel_id=1, source_target_pairs={{0,1},{1,0},{2,3},{3,2},{4,5},{5,4},{6,7},{7,6},{8,9},{9,8},{10,11... | collective-permute-start | bytes 196616 | tf_op jit(solution)/shard_map/ppermute | solution.py:33
  62.9 11.8 %collective-permute-start.28 = (f32[64,256]{1,0:T(8,128)S(1)}, f32[64,256]{1,0:T(8,128)S(1)}, u32[]{:S(2)}, u32[]{:S(2)}) collective-permute-start(f32[64,256]{1,0:T(8,128)S(1)} %get-tuple-element.47), channel_id=1, source_target_pairs={{0,2},{1,3},{2,0},{3,1},{4,6},{5,7},{6,4},{7,5},{8,10},{9,11},{10,... | collective-permute-start | bytes 196616 | tf_op jit(solution)/shard_map/ppermute | solution.py:33
  66.7 8.0 %collective-permute-start.29 = (f32[64,256]{1,0:T(8,128)S(1)}, f32[64,256]{1,0:T(8,128)S(1)}, u32[]{:S(2)}, u32[]{:S(2)}) collective-permute-start(f32[64,256]{1,0:T(8,128)S(1)} %get-tuple-element.47), channel_id=1, source_target_pairs={{0,3},{1,2},{2,1},{3,0},{4,7},{5,6},{6,5},{7,4},{8,11},{9,10},{10,... | collective-permute-start | bytes 196616 | tf_op jit(solution)/shard_map/ppermute | solution.py:33
  68.8 5.8 %collective-permute-start.27 = (f32[64,256]{1,0:T(8,128)S(1)}, f32[64,256]{1,0:T(8,128)S(1)}, u32[]{:S(2)}, u32[]{:S(2)}) collective-permute-start(f32[64,256]{1,0:T(8,128)S(1)} %get-tuple-element.47), channel_id=1, source_target_pairs={{0,1},{1,0},{2,3},{3,2},{4,5},{5,4},{6,7},{7,6},{8,9},{9,8},{10,11... | collective-permute-start | bytes 196616 | tf_op jit(solution)/shard_map/ppermute | solution.py:33
  69.5 10.6 %collective-permute-start.31 = (f32[64,256]{1,0:T(8,128)S(1)}, f32[64,256]{1,0:T(8,128)S(1)}, u32[]{:S(2)}, u32[]{:S(2)}) collective-permute-start(f32[64,256]{1,0:T(8,128)S(1)} %get-tuple-element.48.refs_4_), channel_id=1, source_target_pairs={{0,2},{1,3},{2,0},{3,1},{4,6},{5,7},{6,4},{7,5},{8,10},{9,11},{10,... | collective-permute-start | bytes 196616 | tf_op jit(solution)/shard_map/ppermute | solution.py:33
  72.3 7.8 %collective-permute-start.32 = (f32[64,256]{1,0:T(8,128)S(1)}, f32[64,256]{1,0:T(8,128)S(1)}, u32[]{:S(2)}, u32[]{:S(2)}) collective-permute-start(f32[64,256]{1,0:T(8,128)S(1)} %get-tuple-element.48.refs_4_), channel_id=1, source_target_pairs={{0,3},{1,2},{2,1},{3,0},{4,7},{5,6},{6,5},{7,4},{8,11},{9,10},{10,... | collective-permute-start | bytes 196616 | tf_op jit(solution)/shard_map/ppermute | solution.py:33
  74.6 5.5 %collective-permute-start.30 = (f32[64,256]{1,0:T(8,128)S(1)}, f32[64,256]{1,0:T(8,128)S(1)}, u32[]{:S(2)}, u32[]{:S(2)}) collective-permute-start(f32[64,256]{1,0:T(8,128)S(1)} %get-tuple-element.48.refs_4_), channel_id=1, source_target_pairs={{0,1},{1,0},{2,3},{3,2},{4,5},{5,4},{6,7},{7,6},{8,9},{9,8},{10,11... | collective-permute-start | bytes 196616 | tf_op jit(solution)/shard_map/ppermute | solution.py:33
  75.4 10.4 %collective-permute-start.37 = (f32[64,256]{1,0:T(8,128)S(1)}, f32[64,256]{1,0:T(8,128)S(1)}, u32[]{:S(2)}, u32[]{:S(2)}) collective-permute-start(f32[64,256]{1,0:T(8,128)S(1)} %get-tuple-element.49.refs_5_), channel_id=1, source_target_pairs={{0,2},{1,3},{2,0},{3,1},{4,6},{5,7},{6,4},{7,5},{8,10},{9,11},{10,... | collective-permute-start | bytes 196616 | tf_op jit(solution)/shard_map/ppermute | solution.py:33
  78.0 7.8 %collective-permute-start.38 = (f32[64,256]{1,0:T(8,128)S(1)}, f32[64,256]{1,0:T(8,128)S(1)}, u32[]{:S(2)}, u32[]{:S(2)}) collective-permute-start(f32[64,256]{1,0:T(8,128)S(1)} %get-tuple-element.49.refs_5_), channel_id=1, source_target_pairs={{0,3},{1,2},{2,1},{3,0},{4,7},{5,6},{6,5},{7,4},{8,11},{9,10},{10,... | collective-permute-start | bytes 196616 | tf_op jit(solution)/shard_map/ppermute | solution.py:33
  80.1 5.6 %collective-permute-start.33 = (f32[64,256]{1,0:T(8,128)S(1)}, f32[64,256]{1,0:T(8,128)S(1)}, u32[]{:S(2)}, u32[]{:S(2)}) collective-permute-start(f32[64,256]{1,0:T(8,128)S(1)} %get-tuple-element.49.refs_5_), channel_id=1, source_target_pairs={{0,1},{1,0},{2,3},{3,2},{4,5},{5,4},{6,7},{7,6},{8,9},{9,8},{10,11... | collective-permute-start | bytes 196616 | tf_op jit(solution)/shard_map/ppermute | solution.py:33
  80.9 10.1 %collective-permute-start.35 = (f32[64,256]{1,0:T(8,128)S(1)}, f32[64,256]{1,0:T(8,128)S(1)}, u32[]{:S(2)}, u32[]{:S(2)}) collective-permute-start(f32[64,256]{1,0:T(8,128)S(1)} %get-tuple-element.50), channel_id=1, source_target_pairs={{0,2},{1,3},{2,0},{3,1},{4,6},{5,7},{6,4},{7,5},{8,10},{9,11},{10,... | collective-permute-start | bytes 196616 | tf_op jit(solution)/shard_map/ppermute | solution.py:33
  83.6 12.6 %collective-permute-start.36 = (f32[64,256]{1,0:T(8,128)S(1)}, f32[64,256]{1,0:T(8,128)S(1)}, u32[]{:S(2)}, u32[]{:S(2)}) collective-permute-start(f32[64,256]{1,0:T(8,128)S(1)} %get-tuple-element.50), channel_id=1, source_target_pairs={{0,3},{1,2},{2,1},{3,0},{4,7},{5,6},{6,5},{7,4},{8,11},{9,10},{10,... | collective-permute-start | bytes 196616 | tf_op jit(solution)/shard_map/ppermute | solution.py:33
  85.8 5.2 %collective-permute-start.34 = (f32[64,256]{1,0:T(8,128)S(1)}, f32[64,256]{1,0:T(8,128)S(1)}, u32[]{:S(2)}, u32[]{:S(2)}) collective-permute-start(f32[64,256]{1,0:T(8,128)S(1)} %get-tuple-element.50), channel_id=1, source_target_pairs={{0,1},{1,0},{2,3},{3,2},{4,5},{5,4},{6,7},{7,6},{8,9},{9,8},{10,11... | collective-permute-start | bytes 196616 | tf_op jit(solution)/shard_map/ppermute | solution.py:33
  86.5 9.7 %collective-permute-start.40 = (f32[64,256]{1,0:T(8,128)S(1)}, f32[64,256]{1,0:T(8,128)S(1)}, u32[]{:S(2)}, u32[]{:S(2)}) collective-permute-start(f32[64,256]{1,0:T(8,128)S(1)} %get-tuple-element.51), channel_id=1, source_target_pairs={{0,2},{1,3},{2,0},{3,1},{4,6},{5,7},{6,4},{7,5},{8,10},{9,11},{10,... | collective-permute-start | bytes 196616 | tf_op jit(solution)/shard_map/ppermute | solution.py:33
  89.2 7.0 %collective-permute-start.41 = (f32[64,256]{1,0:T(8,128)S(1)}, f32[64,256]{1,0:T(8,128)S(1)}, u32[]{:S(2)}, u32[]{:S(2)}) collective-permute-start(f32[64,256]{1,0:T(8,128)S(1)} %get-tuple-element.51), channel_id=1, source_target_pairs={{0,3},{1,2},{2,1},{3,0},{4,7},{5,6},{6,5},{7,4},{8,11},{9,10},{10,... | collective-permute-start | bytes 196616 | tf_op jit(solution)/shard_map/ppermute | solution.py:33
  91.0 5.2 %collective-permute-start.39 = (f32[64,256]{1,0:T(8,128)S(1)}, f32[64,256]{1,0:T(8,128)S(1)}, u32[]{:S(2)}, u32[]{:S(2)}) collective-permute-start(f32[64,256]{1,0:T(8,128)S(1)} %get-tuple-element.51), channel_id=1, source_target_pairs={{0,1},{1,0},{2,3},{3,2},{4,5},{5,4},{6,7},{7,6},{8,9},{9,8},{10,11... | collective-permute-start | bytes 196616 | tf_op jit(solution)/shard_map/ppermute | solution.py:33
  96.9 9.3 %collective-permute-start.43 = (f32[64,256]{1,0:T(8,128)S(1)}, f32[64,256]{1,0:T(8,128)S(1)}, u32[]{:S(2)}, u32[]{:S(2)}) collective-permute-start(f32[64,256]{1,0:T(8,128)S(1)} %get-tuple-element.52.refs_6_), channel_id=1, source_target_pairs={{0,2},{1,3},{2,0},{3,1},{4,6},{5,7},{6,4},{7,5},{8,10},{9,11},{10,... | collective-permute-start | bytes 196616 | tf_op jit(solution)/shard_map/ppermute | solution.py:33
  99.3 7.1 %collective-permute-start.44 = (f32[64,256]{1,0:T(8,128)S(1)}, f32[64,256]{1,0:T(8,128)S(1)}, u32[]{:S(2)}, u32[]{:S(2)}) collective-permute-start(f32[64,256]{1,0:T(8,128)S(1)} %get-tuple-element.52.refs_6_), channel_id=1, source_target_pairs={{0,3},{1,2},{2,1},{3,0},{4,7},{5,6},{6,5},{7,4},{8,11},{9,10},{10,... | collective-permute-start | bytes 196616 | tf_op jit(solution)/shard_map/ppermute | solution.py:33
  101.2 5.1 %collective-permute-start.42 = (f32[64,256]{1,0:T(8,128)S(1)}, f32[64,256]{1,0:T(8,128)S(1)}, u32[]{:S(2)}, u32[]{:S(2)}) collective-permute-start(f32[64,256]{1,0:T(8,128)S(1)} %get-tuple-element.52.refs_6_), channel_id=1, source_target_pairs={{0,1},{1,0},{2,3},{3,2},{4,5},{5,4},{6,7},{7,6},{8,9},{9,8},{10,11... | collective-permute-start | bytes 196616 | tf_op jit(solution)/shard_map/ppermute | solution.py:33
  101.8 9.3 %collective-permute-start.46 = (f32[64,256]{1,0:T(8,128)S(1)}, f32[64,256]{1,0:T(8,128)S(1)}, u32[]{:S(2)}, u32[]{:S(2)}) collective-permute-start(f32[64,256]{1,0:T(8,128)S(1)} %get-tuple-element.53.refs_7_), channel_id=1, source_target_pairs={{0,2},{1,3},{2,0},{3,1},{4,6},{5,7},{6,4},{7,5},{8,10},{9,11},{10,... | collective-permute-start | bytes 196616 | tf_op jit(solution)/shard_map/ppermute | solution.py:33
  104.4 6.8 %collective-permute-start.47 = (f32[64,256]{1,0:T(8,128)S(1)}, f32[64,256]{1,0:T(8,128)S(1)}, u32[]{:S(2)}, u32[]{:S(2)}) collective-permute-start(f32[64,256]{1,0:T(8,128)S(1)} %get-tuple-element.53.refs_7_), channel_id=1, source_target_pairs={{0,3},{1,2},{2,1},{3,0},{4,7},{5,6},{6,5},{7,4},{8,11},{9,10},{10,... | collective-permute-start | bytes 196616 | tf_op jit(solution)/shard_map/ppermute | solution.py:33
  106.3 4.9 %collective-permute-start.45 = (f32[64,256]{1,0:T(8,128)S(1)}, f32[64,256]{1,0:T(8,128)S(1)}, u32[]{:S(2)}, u32[]{:S(2)}) collective-permute-start(f32[64,256]{1,0:T(8,128)S(1)} %get-tuple-element.53.refs_7_), channel_id=1, source_target_pairs={{0,1},{1,0},{2,3},{3,2},{4,5},{5,4},{6,7},{7,6},{8,9},{9,8},{10,11... | collective-permute-start | bytes 196616 | tf_op jit(solution)/shard_map/ppermute | solution.py:33
  106.4 20.6 %copy-start.3 = (f32[2,256,1024]{2,1,0:T(8,128)S(1)}, f32[2,256,1024]{2,1,0:T(8,128)}, u32[]{:S(2)}) copy-start(f32[2,256,1024]{2,1,0:T(8,128)} %refs_0_.1) | copy-start | bytes 6291460
  106.4 20.6 %copy-start.4 = (f32[1,256,1024]{2,1,0:T(8,128)S(1)}, f32[1,256,1024]{2,1,0:T(8,128)}, u32[]{:S(2)}) copy-start(f32[1,256,1024]{2,1,0:T(8,128)} %refs_1_.1) | copy-start | bytes 3145732
  112.4 1.4 collective-permute-start.48
  113.9 4.6 %collective-permute-start.49 = (f32[2,16,512]{2,1,0:T(8,128)S(1)}, f32[2,16,512]{2,1,0:T(8,128)S(1)}, u32[]{:S(2)}, u32[]{:S(2)}) collective-permute-start(f32[2,16,512]{2,1,0:T(8,128)S(1)} %get-tuple-element.58), channel_id=1, source_target_pairs={{0,8},{4,12},{8,0},{12,4},{16,24},{20,28},{24,16},{28,20},{1,9},{5... | collective-permute-start | bytes 196616 | tf_op jit(solution)/shard_map/ppermute | solution.py:74
  115.4 4.3 %collective-permute-start.50 = (f32[2,16,512]{2,1,0:T(8,128)S(1)}, f32[2,16,512]{2,1,0:T(8,128)S(1)}, u32[]{:S(2)}, u32[]{:S(2)}) collective-permute-start(f32[2,16,512]{2,1,0:T(8,128)S(1)} %get-tuple-element.59), channel_id=1, source_target_pairs={{0,16},{4,20},{8,24},{12,28},{16,0},{20,4},{24,8},{28,12},{1,17},{... | collective-permute-start | bytes 196616 | tf_op jit(solution)/shard_map/ppermute | solution.py:74
  116.9 5.2 %collective-permute-start.51 = (f32[2,16,512]{2,1,0:T(8,128)S(1)}, f32[2,16,512]{2,1,0:T(8,128)S(1)}, u32[]{:S(2)}, u32[]{:S(2)}) collective-permute-start(f32[2,16,512]{2,1,0:T(8,128)S(1)} %get-tuple-element.60), channel_id=1, source_target_pairs={{0,24},{4,28},{8,16},{12,20},{16,8},{20,12},{24,0},{28,4},{1,25},{... | collective-permute-start | bytes 196616 | tf_op jit(solution)/shard_map/ppermute | solution.py:74
  122.5 4.9 %collective-permute-start.52 = (f32[16,1280]{1,0:T(8,128)S(1)}, f32[16,1280]{1,0:T(8,128)S(1)}, u32[]{:S(2)}, u32[]{:S(2)}) collective-permute-start(f32[16,1280]{1,0:T(8,128)S(1)} %get-tuple-element.63), channel_id=1, source_target_pairs={{0,1},{1,0},{2,3},{3,2},{4,5},{5,4},{6,7},{7,6},{8,9},{9,8},{10,11... | collective-permute-start | bytes 245768 | tf_op jit(solution)/shard_map/ppermute | solution.py:33
  122.7 7.2 %collective-permute-start.53 = (f32[16,1280]{1,0:T(8,128)S(1)}, f32[16,1280]{1,0:T(8,128)S(1)}, u32[]{:S(2)}, u32[]{:S(2)}) collective-permute-start(f32[16,1280]{1,0:T(8,128)S(1)} %get-tuple-element.64), channel_id=1, source_target_pairs={{0,2},{1,3},{2,0},{3,1},{4,6},{5,7},{6,4},{7,5},{8,10},{9,11},{10,... | collective-permute-start | bytes 245768 | tf_op jit(solution)/shard_map/ppermute | solution.py:33
  125.1 6.4 %collective-permute-start.54 = (f32[16,1280]{1,0:T(8,128)S(1)}, f32[16,1280]{1,0:T(8,128)S(1)}, u32[]{:S(2)}, u32[]{:S(2)}) collective-permute-start(f32[16,1280]{1,0:T(8,128)S(1)} %get-tuple-element.65), channel_id=1, source_target_pairs={{0,3},{1,2},{2,1},{3,0},{4,7},{5,6},{6,5},{7,4},{8,11},{9,10},{10,... | collective-permute-start | bytes 245768 | tf_op jit(solution)/shard_map/ppermute | solution.py:33
  131.8 4.4 %collective-permute-start.55 = (f32[16,256]{1,0:T(8,128)S(1)}, f32[16,256]{1,0:T(8,128)S(1)}, u32[]{:S(2)}, u32[]{:S(2)}) collective-permute-start(f32[16,256]{1,0:T(8,128)S(1)} %get-tuple-element.68.refs_0_.refs_6_), channel_id=1, source_target_pairs={{0,1},{1,0},{2,3},{3,2},{4,5},{5,4},{6,7},{7,6},{8,9},{9,8},{10,11... | collective-permute-start | bytes 49160 | tf_op jit(solution)/shard_map/ppermute | solution.py:33
  132.6 4.6 %collective-permute-start.56 = (f32[16,256]{1,0:T(8,128)S(1)}, f32[16,256]{1,0:T(8,128)S(1)}, u32[]{:S(2)}, u32[]{:S(2)}) collective-permute-start(f32[16,256]{1,0:T(8,128)S(1)} %get-tuple-element.68.refs_0_.refs_6_), channel_id=1, source_target_pairs={{0,2},{1,3},{2,0},{3,1},{4,6},{5,7},{6,4},{7,5},{8,10},{9,11},{10,... | collective-permute-start | bytes 49160 | tf_op jit(solution)/shard_map/ppermute | solution.py:33
  134.3 5.6 %collective-permute-start.57 = (f32[16,256]{1,0:T(8,128)S(1)}, f32[16,256]{1,0:T(8,128)S(1)}, u32[]{:S(2)}, u32[]{:S(2)}) collective-permute-start(f32[16,256]{1,0:T(8,128)S(1)} %get-tuple-element.68.refs_0_.refs_6_), channel_id=1, source_target_pairs={{0,3},{1,2},{2,1},{3,0},{4,7},{5,6},{6,5},{7,4},{8,11},{9,10},{10,... | collective-permute-start | bytes 49160 | tf_op jit(solution)/shard_map/ppermute | solution.py:33
  140.2 4.4 %collective-permute-start.58 = (f32[16,256]{1,0:T(8,128)S(1)}, f32[16,256]{1,0:T(8,128)S(1)}, u32[]{:S(2)}, u32[]{:S(2)}) collective-permute-start(f32[16,256]{1,0:T(8,128)S(1)} %shard_map.124.refs_0_), channel_id=1, source_target_pairs={{0,1},{1,0},{2,3},{3,2},{4,5},{5,4},{6,7},{7,6},{8,9},{9,8},{10,11... | collective-permute-start | bytes 49160 | tf_op jit(solution)/shard_map/ppermute | solution.py:33
  140.3 4.7 %collective-permute-start.59 = (f32[16,256]{1,0:T(8,128)S(1)}, f32[16,256]{1,0:T(8,128)S(1)}, u32[]{:S(2)}, u32[]{:S(2)}) collective-permute-start(f32[16,256]{1,0:T(8,128)S(1)} %shard_map.124.refs_0_), channel_id=1, source_target_pairs={{0,2},{1,3},{2,0},{3,1},{4,6},{5,7},{6,4},{7,5},{8,10},{9,11},{10,... | collective-permute-start | bytes 49160 | tf_op jit(solution)/shard_map/ppermute | solution.py:33
  142.8 5.5 %collective-permute-start.60 = (f32[16,256]{1,0:T(8,128)S(1)}, f32[16,256]{1,0:T(8,128)S(1)}, u32[]{:S(2)}, u32[]{:S(2)}) collective-permute-start(f32[16,256]{1,0:T(8,128)S(1)} %shard_map.124.refs_0_), channel_id=1, source_target_pairs={{0,3},{1,2},{2,1},{3,0},{4,7},{5,6},{6,5},{7,4},{8,11},{9,10},{10,... | collective-permute-start | bytes 49160 | tf_op jit(solution)/shard_map/ppermute | solution.py:33
  (7 other events, 93.3 us)

commit v17 on v16

--- a/solution.py
+++ b/solution.py
@@ -450,8 +450,12 @@
     for step in range(2 * supernodes):
         current = step // 2
         for i in range(streams):
-            ties = [(1, last[1][1])] if last is not None else []
+            turn_taken = step > 0 and last is not None
+            ties = [(1, last[0][1][1])] if step * streams + i > streams else []
             pieces = gather_rows(values[i], ties)
+            if turn_taken and True:
+                offset, piece = pieces[1]
+                pieces[1] = (offset, lax.optimization_barrier((piece, last[1]))[0])
             if step == 0:
                 owned = apply_split([p for _, p in pieces], first_top, first_rest, 0)
             else:
@@ -465,7 +469,7 @@
             else:
                 gathered[current][i] = whole
             values[i] = owned
-            last = pieces
+            last = (pieces, owned)
 
     by_stream = [[values[i] for values in gathered] for i in range(streams)]
     done = [tile_terms(values, tiles[0, 0], tile_source) for values in by_stream[:-1]]

time: 150 us -> 139 us (0.927)
  waiting for transfers between devices: 39.1 us -> 22.1 us
  starting transfers between devices: 88.8 us -> 95.6 us
    ppermute x57, waiting for transfers between devices: 34 us -> 17.1 us  [send(): return lax.ppermute(value, axis, pairs)]
    ppermute x57, starting transfers between devices: 85.2 us -> 92 us  [send(): return lax.ppermute(value, axis, pairs)]
  transfers between devices with their start and end apart: 61 -> 61, of which waited for: 22 -> 14; matrix products, arithmetic and copies ran while one was open for 6% -> 7% of each run, Pallas kernels for 3% -> 3%
where the time goes in v17:
time: 139 us
  starting transfers between devices  95.6 us (69%)
  waiting for transfers between devices  22.1 us (16%)
  matrix products  7.53 us (5%)
  Pallas kernels  7.51 us (5%)
  local copies, waits for them, and re-layouts  2.84 us (2%)
  between operations  2.17 us (2%)
  other arithmetic  1.41 us (1%)
    ppermute x57, starting transfers between devices, send(): return lax.ppermute(value, axis, pairs)  92 us
    ppermute x57, waiting for transfers between devices, send(): return lax.ppermute(value, axis, pairs)  17.1 us
    dot_general x12, matrix products, contract_last(): lax.dot_general(left, right, (((left.ndim - 1,), (right.ndim - 1,)), ((),...  7.53 us
    pallas_call x13, Pallas kernels, local_kernel(): pl.pallas_call(body, out_shape=list(outs), in_specs=specs or [VMEM] * len...  7.51 us
    ppermute x3, waiting for transfers between devices, swap(): return lax.ppermute(value, axis, pairs)  3.69 us
    ppermute x3, starting transfers between devices, swap(): return lax.ppermute(value, axis, pairs)  3.55 us
  transfers between devices with their start and end apart: 61, of which 14 were waited for; matrix products, arithmetic and copies ran while one was open for 7% of the time, Pallas kernels for 3%

profile of v17, /device:TPU:0, one launch (start us, length us, event | category | flops | bytes accessed | tf_op | source)
XLA Modules:
  0.0 139.2 jit_solution(14490074010744265786)
XLA Ops:
  0.6 1.0 copy-done.1
  1.9 3.1 %collective-permute-start = (f32[64,256]{1,0:T(8,128)S(1)}, f32[64,256]{1,0:T(8,128)S(1)}, u32[]{:S(2)}, u32[]{:S(2)}) collective-permute-start(f32[64,256]{1,0:T(8,128)S(1)} %get-tuple-element.49.refs_0_), channel_id=1, source_target_pairs={{0,1},{1,0},{2,3},{3,2},{4,5},{5,4},{6,7},{7,6},{8,9},{9,8},{10,11... | collective-permute-start | bytes 196616 | tf_op jit(solution)/shard_map/ppermute | solution.py:33
  5.0 2.6 %collective-permute-start.1 = (f32[64,256]{1,0:T(8,128)S(1)}, f32[64,256]{1,0:T(8,128)S(1)}, u32[]{:S(2)}, u32[]{:S(2)}) collective-permute-start(f32[64,256]{1,0:T(8,128)S(1)} %get-tuple-element.49.refs_0_), channel_id=1, source_target_pairs={{0,2},{1,3},{2,0},{3,1},{4,6},{5,7},{6,4},{7,5},{8,10},{9,11},{10,... | collective-permute-start | bytes 196616 | tf_op jit(solution)/shard_map/ppermute | solution.py:33
  7.6 0.9 collective-permute-start.3
  8.5 3.5 %collective-permute-start.4 = (f32[64,256]{1,0:T(8,128)S(1)}, f32[64,256]{1,0:T(8,128)S(1)}, u32[]{:S(2)}, u32[]{:S(2)}) collective-permute-start(f32[64,256]{1,0:T(8,128)S(1)} %get-tuple-element.50.refs_0_), channel_id=1, source_target_pairs={{0,2},{1,3},{2,0},{3,1},{4,6},{5,7},{6,4},{7,5},{8,10},{9,11},{10,... | collective-permute-start | bytes 196616 | tf_op jit(solution)/shard_map/ppermute | solution.py:33
  12.0 1.4 %fusion = (bf16[1,256,1024]{2,1,0:T(8,128)(2,1)S(1)}, bf16[1,256,1024]{2,1,0:T(8,128)(2,1)S(1)}) fusion(f32[1,4,256,1024]{3,2,1,0:T(8,128)} %param.11), kind=kLoop, calls=%fused_computation.8 | loop fusion | flops 1048576 | bytes 2097152 | tf_op jit(solution)/shard_map/convert_element_type | solution.py:445
  13.4 1.0 copy-done.2
  16.0 1.8 %collective-permute-start.6 = (f32[64,256]{1,0:T(8,128)S(1)}, f32[64,256]{1,0:T(8,128)S(1)}, u32[]{:S(2)}, u32[]{:S(2)}) collective-permute-start(f32[64,256]{1,0:T(8,128)S(1)} %shard_map.114.refs_0_), channel_id=1, source_target_pairs={{0,1},{1,0},{2,3},{3,2},{4,5},{5,4},{6,7},{7,6},{8,9},{9,8},{10,11... | collective-permute-start | bytes 196616 | tf_op jit(solution)/shard_map/ppermute | solution.py:33
  17.8 2.6 %collective-permute-start.7 = (f32[64,256]{1,0:T(8,128)S(1)}, f32[64,256]{1,0:T(8,128)S(1)}, u32[]{:S(2)}, u32[]{:S(2)}) collective-permute-start(f32[64,256]{1,0:T(8,128)S(1)} %shard_map.114.refs_0_), channel_id=1, source_target_pairs={{0,2},{1,3},{2,0},{3,1},{4,6},{5,7},{6,4},{7,5},{8,10},{9,11},{10,... | collective-permute-start | bytes 196616 | tf_op jit(solution)/shard_map/ppermute | solution.py:33
  20.4 0.8 collective-permute-start.8
  21.7 2.1 %collective-permute-start.11 = (f32[64,256]{1,0:T(8,128)S(1)}, f32[64,256]{1,0:T(8,128)S(1)}, u32[]{:S(2)}, u32[]{:S(2)}) collective-permute-start(f32[64,256]{1,0:T(8,128)S(1)} %shard_map.115.refs_1_), channel_id=1, source_target_pairs={{0,2},{1,3},{2,0},{3,1},{4,6},{5,7},{6,4},{7,5},{8,10},{9,11},{10,... | collective-permute-start | bytes 196616 | tf_op jit(solution)/shard_map/ppermute | solution.py:33
  23.8 1.1 collective-permute-start.12
  25.5 1.6 %collective-permute-done.7 = f32[64,256]{1,0:T(8,128)S(1)} collective-permute-done((f32[64,256]{1,0:T(8,128)S(1)}, f32[64,256]{1,0:T(8,128)S(1)}, u32[]{:S(2)}, u32[]{:S(2)}) %collective-permute-start.7) | collective-permute-done | bytes 65568 | tf_op jit(solution)/shard_map/ppermute | solution.py:33
  28.0 5.3 %collective-permute-start.13 = (f32[64,256]{1,0:T(8,128)S(1)}, f32[64,256]{1,0:T(8,128)S(1)}, u32[]{:S(2)}, u32[]{:S(2)}) collective-permute-start(f32[64,256]{1,0:T(8,128)S(1)} %get-tuple-element.54), channel_id=1, source_target_pairs={{0,2},{1,3},{2,0},{3,1},{4,6},{5,7},{6,4},{7,5},{8,10},{9,11},{10,... | collective-permute-start | bytes 196616 | tf_op jit(solution)/shard_map/ppermute | solution.py:33
  33.3 1.8 %collective-permute-start.14 = (f32[64,256]{1,0:T(8,128)S(1)}, f32[64,256]{1,0:T(8,128)S(1)}, u32[]{:S(2)}, u32[]{:S(2)}) collective-permute-start(f32[64,256]{1,0:T(8,128)S(1)} %get-tuple-element.54), channel_id=1, source_target_pairs={{0,3},{1,2},{2,1},{3,0},{4,7},{5,6},{6,5},{7,4},{8,11},{9,10},{10,... | collective-permute-start | bytes 196616 | tf_op jit(solution)/shard_map/ppermute | solution.py:33
  35.8 2.6 %collective-permute-start.16 = (f32[64,256]{1,0:T(8,128)S(1)}, f32[64,256]{1,0:T(8,128)S(1)}, u32[]{:S(2)}, u32[]{:S(2)}) collective-permute-start(f32[64,256]{1,0:T(8,128)S(1)} %get-tuple-element.56), channel_id=1, source_target_pairs={{0,2},{1,3},{2,0},{3,1},{4,6},{5,7},{6,4},{7,5},{8,10},{9,11},{10,... | collective-permute-start | bytes 196616 | tf_op jit(solution)/shard_map/ppermute | solution.py:33
  38.5 1.8 %collective-permute-start.17 = (f32[64,256]{1,0:T(8,128)S(1)}, f32[64,256]{1,0:T(8,128)S(1)}, u32[]{:S(2)}, u32[]{:S(2)}) collective-permute-start(f32[64,256]{1,0:T(8,128)S(1)} %get-tuple-element.56), channel_id=1, source_target_pairs={{0,3},{1,2},{2,1},{3,0},{4,7},{5,6},{6,5},{7,4},{8,11},{9,10},{10,... | collective-permute-start | bytes 196616 | tf_op jit(solution)/shard_map/ppermute | solution.py:33
  41.1 2.6 %collective-permute-start.19 = (f32[64,256]{1,0:T(8,128)S(1)}, f32[64,256]{1,0:T(8,128)S(1)}, u32[]{:S(2)}, u32[]{:S(2)}) collective-permute-start(f32[64,256]{1,0:T(8,128)S(1)} %get-tuple-element.58.refs_2_), channel_id=1, source_target_pairs={{0,2},{1,3},{2,0},{3,1},{4,6},{5,7},{6,4},{7,5},{8,10},{9,11},{10,... | collective-permute-start | bytes 196616 | tf_op jit(solution)/shard_map/ppermute | solution.py:33
  43.8 1.8 %collective-permute-start.20 = (f32[64,256]{1,0:T(8,128)S(1)}, f32[64,256]{1,0:T(8,128)S(1)}, u32[]{:S(2)}, u32[]{:S(2)}) collective-permute-start(f32[64,256]{1,0:T(8,128)S(1)} %get-tuple-element.58.refs_2_), channel_id=1, source_target_pairs={{0,3},{1,2},{2,1},{3,0},{4,7},{5,6},{6,5},{7,4},{8,11},{9,10},{10,... | collective-permute-start | bytes 196616 | tf_op jit(solution)/shard_map/ppermute | solution.py:33
  46.6 3.2 %collective-permute-start.23 = (f32[64,256]{1,0:T(8,128)S(1)}, f32[64,256]{1,0:T(8,128)S(1)}, u32[]{:S(2)}, u32[]{:S(2)}) collective-permute-start(f32[64,256]{1,0:T(8,128)S(1)} %get-tuple-element.60.refs_3_), channel_id=1, source_target_pairs={{0,2},{1,3},{2,0},{3,1},{4,6},{5,7},{6,4},{7,5},{8,10},{9,11},{10,... | collective-permute-start | bytes 196616 | tf_op jit(solution)/shard_map/ppermute | solution.py:33
  49.9 1.1 collective-permute-start.24
  51.1 0.6 constant_dynamic-update-slice_fusion.35
  51.8 3.3 %collective-permute-start.25 = (f32[64,256]{1,0:T(8,128)S(1)}, f32[64,256]{1,0:T(8,128)S(1)}, u32[]{:S(2)}, u32[]{:S(2)}) collective-permute-start(f32[64,256]{1,0:T(8,128)S(1)} %get-tuple-element.62), channel_id=1, source_target_pairs={{0,2},{1,3},{2,0},{3,1},{4,6},{5,7},{6,4},{7,5},{8,10},{9,11},{10,... | collective-permute-start | bytes 196616 | tf_op jit(solution)/shard_map/ppermute | solution.py:33
  55.0 1.8 %collective-permute-start.26 = (f32[64,256]{1,0:T(8,128)S(1)}, f32[64,256]{1,0:T(8,128)S(1)}, u32[]{:S(2)}, u32[]{:S(2)}) collective-permute-start(f32[64,256]{1,0:T(8,128)S(1)} %get-tuple-element.62), channel_id=1, source_target_pairs={{0,3},{1,2},{2,1},{3,0},{4,7},{5,6},{6,5},{7,4},{8,11},{9,10},{10,... | collective-permute-start | bytes 196616 | tf_op jit(solution)/shard_map/ppermute | solution.py:33
  57.0 0.6 constant_dynamic-update-slice_fusion.27
  57.6 3.5 %collective-permute-start.28 = (f32[64,256]{1,0:T(8,128)S(1)}, f32[64,256]{1,0:T(8,128)S(1)}, u32[]{:S(2)}, u32[]{:S(2)}) collective-permute-start(f32[64,256]{1,0:T(8,128)S(1)} %get-tuple-element.64), channel_id=1, source_target_pairs={{0,2},{1,3},{2,0},{3,1},{4,6},{5,7},{6,4},{7,5},{8,10},{9,11},{10,... | collective-permute-start | bytes 196616 | tf_op jit(solution)/shard_map/ppermute | solution.py:33
  61.1 1.1 collective-permute-start.29
  62.9 3.3 %collective-permute-start.31 = (f32[64,256]{1,0:T(8,128)S(1)}, f32[64,256]{1,0:T(8,128)S(1)}, u32[]{:S(2)}, u32[]{:S(2)}) collective-permute-start(f32[64,256]{1,0:T(8,128)S(1)} %get-tuple-element.66.refs_4_), channel_id=1, source_target_pairs={{0,2},{1,3},{2,0},{3,1},{4,6},{5,7},{6,4},{7,5},{8,10},{9,11},{10,... | collective-permute-start | bytes 196616 | tf_op jit(solution)/shard_map/ppermute | solution.py:33
  66.3 1.8 %collective-permute-start.32 = (f32[64,256]{1,0:T(8,128)S(1)}, f32[64,256]{1,0:T(8,128)S(1)}, u32[]{:S(2)}, u32[]{:S(2)}) collective-permute-start(f32[64,256]{1,0:T(8,128)S(1)} %get-tuple-element.66.refs_4_), channel_id=1, source_target_pairs={{0,3},{1,2},{2,1},{3,0},{4,7},{5,6},{6,5},{7,4},{8,11},{9,10},{10,... | collective-permute-start | bytes 196616 | tf_op jit(solution)/shard_map/ppermute | solution.py:33
  68.8 2.8 %collective-permute-start.35 = (f32[64,256]{1,0:T(8,128)S(1)}, f32[64,256]{1,0:T(8,128)S(1)}, u32[]{:S(2)}, u32[]{:S(2)}) collective-permute-start(f32[64,256]{1,0:T(8,128)S(1)} %get-tuple-element.68.refs_5_), channel_id=1, source_target_pairs={{0,2},{1,3},{2,0},{3,1},{4,6},{5,7},{6,4},{7,5},{8,10},{9,11},{10,... | collective-permute-start | bytes 196616 | tf_op jit(solution)/shard_map/ppermute | solution.py:33
  71.7 1.7 %collective-permute-start.36 = (f32[64,256]{1,0:T(8,128)S(1)}, f32[64,256]{1,0:T(8,128)S(1)}, u32[]{:S(2)}, u32[]{:S(2)}) collective-permute-start(f32[64,256]{1,0:T(8,128)S(1)} %get-tuple-element.68.refs_5_), channel_id=1, source_target_pairs={{0,3},{1,2},{2,1},{3,0},{4,7},{5,6},{6,5},{7,4},{8,11},{9,10},{10,... | collective-permute-start | bytes 196616 | tf_op jit(solution)/shard_map/ppermute | solution.py:33
  73.6 0.6 constant_dynamic-update-slice_fusion.19
  74.2 3.7 %collective-permute-start.37 = (f32[64,256]{1,0:T(8,128)S(1)}, f32[64,256]{1,0:T(8,128)S(1)}, u32[]{:S(2)}, u32[]{:S(2)}) collective-permute-start(f32[64,256]{1,0:T(8,128)S(1)} %get-tuple-element.70), channel_id=1, source_target_pairs={{0,2},{1,3},{2,0},{3,1},{4,6},{5,7},{6,4},{7,5},{8,10},{9,11},{10,... | collective-permute-start | bytes 196616 | tf_op jit(solution)/shard_map/ppermute | solution.py:33
  77.9 1.4 %collective-permute-start.38 = (f32[64,256]{1,0:T(8,128)S(1)}, f32[64,256]{1,0:T(8,128)S(1)}, u32[]{:S(2)}, u32[]{:S(2)}) collective-permute-start(f32[64,256]{1,0:T(8,128)S(1)} %get-tuple-element.70), channel_id=1, source_target_pairs={{0,3},{1,2},{2,1},{3,0},{4,7},{5,6},{6,5},{7,4},{8,11},{9,10},{10,... | collective-permute-start | bytes 196616 | tf_op jit(solution)/shard_map/ppermute | solution.py:33
  79.5 0.6 constant_dynamic-update-slice_fusion.11
  80.2 3.0 %collective-permute-start.40 = (f32[64,256]{1,0:T(8,128)S(1)}, f32[64,256]{1,0:T(8,128)S(1)}, u32[]{:S(2)}, u32[]{:S(2)}) collective-permute-start(f32[64,256]{1,0:T(8,128)S(1)} %get-tuple-element.72), channel_id=1, source_target_pairs={{0,2},{1,3},{2,0},{3,1},{4,6},{5,7},{6,4},{7,5},{8,10},{9,11},{10,... | collective-permute-start | bytes 196616 | tf_op jit(solution)/shard_map/ppermute | solution.py:33
  83.2 1.5 %collective-permute-start.41 = (f32[64,256]{1,0:T(8,128)S(1)}, f32[64,256]{1,0:T(8,128)S(1)}, u32[]{:S(2)}, u32[]{:S(2)}) collective-permute-start(f32[64,256]{1,0:T(8,128)S(1)} %get-tuple-element.72), channel_id=1, source_target_pairs={{0,3},{1,2},{2,1},{3,0},{4,7},{5,6},{6,5},{7,4},{8,11},{9,10},{10,... | collective-permute-start | bytes 196616 | tf_op jit(solution)/shard_map/ppermute | solution.py:33
  85.6 3.0 %collective-permute-start.43 = (f32[64,256]{1,0:T(8,128)S(1)}, f32[64,256]{1,0:T(8,128)S(1)}, u32[]{:S(2)}, u32[]{:S(2)}) collective-permute-start(f32[64,256]{1,0:T(8,128)S(1)} %get-tuple-element.74.refs_6_), channel_id=1, source_target_pairs={{0,2},{1,3},{2,0},{3,1},{4,6},{5,7},{6,4},{7,5},{8,10},{9,11},{10,... | collective-permute-start | bytes 196616 | tf_op jit(solution)/shard_map/ppermute | solution.py:33
  88.5 2.1 %collective-permute-start.44 = (f32[64,256]{1,0:T(8,128)S(1)}, f32[64,256]{1,0:T(8,128)S(1)}, u32[]{:S(2)}, u32[]{:S(2)}) collective-permute-start(f32[64,256]{1,0:T(8,128)S(1)} %get-tuple-element.74.refs_6_), channel_id=1, source_target_pairs={{0,3},{1,2},{2,1},{3,0},{4,7},{5,6},{6,5},{7,4},{8,11},{9,10},{10,... | collective-permute-start | bytes 196616 | tf_op jit(solution)/shard_map/ppermute | solution.py:33
  91.4 3.4 %collective-permute-start.46 = (f32[64,256]{1,0:T(8,128)S(1)}, f32[64,256]{1,0:T(8,128)S(1)}, u32[]{:S(2)}, u32[]{:S(2)}) collective-permute-start(f32[64,256]{1,0:T(8,128)S(1)} %get-tuple-element.76.refs_7_), channel_id=1, source_target_pairs={{0,2},{1,3},{2,0},{3,1},{4,6},{5,7},{6,4},{7,5},{8,10},{9,11},{10,... | collective-permute-start | bytes 196616 | tf_op jit(solution)/shard_map/ppermute | solution.py:33
  94.8 1.0 collective-permute-start.47
  96.0 1.2 shard_map.117.refs_0_
  97.2 2.9 %collective-permute-done.45 = f32[64,256]{1,0:T(8,128)S(1)} collective-permute-done((f32[64,256]{1,0:T(8,128)S(1)}, f32[64,256]{1,0:T(8,128)S(1)}, u32[]{:S(2)}, u32[]{:S(2)}) %collective-permute-start.45) | collective-permute-done | bytes 65568 | tf_op jit(solution)/shard_map/ppermute | solution.py:33
  100.2 0.7 collective-permute-done.47
  100.9 1.2 shard_map.118
  102.2 1.3 collective-permute-done.48.refs_1_
  103.5 1.6 %collective-permute-start.49 = (f32[2,16,512]{2,1,0:T(8,128)S(1)}, f32[2,16,512]{2,1,0:T(8,128)S(1)}, u32[]{:S(2)}, u32[]{:S(2)}) collective-permute-start(f32[2,16,512]{2,1,0:T(8,128)S(1)} %get-tuple-element.82), channel_id=1, source_target_pairs={{0,8},{4,12},{8,0},{12,4},{16,24},{20,28},{24,16},{28,20},{1,9},{5... | collective-permute-start | bytes 196616 | tf_op jit(solution)/shard_map/ppermute | solution.py:74
  105.1 1.5 %collective-permute-start.50 = (f32[2,16,512]{2,1,0:T(8,128)S(1)}, f32[2,16,512]{2,1,0:T(8,128)S(1)}, u32[]{:S(2)}, u32[]{:S(2)}) collective-permute-start(f32[2,16,512]{2,1,0:T(8,128)S(1)} %get-tuple-element.83), channel_id=1, source_target_pairs={{0,16},{4,20},{8,24},{12,28},{16,0},{20,4},{24,8},{28,12},{1,17},{... | collective-permute-start | bytes 196616 | tf_op jit(solution)/shard_map/ppermute | solution.py:74
  107.1 1.0 shard_map.119
  108.1 1.3 collective-permute-done.50.refs_2_
  109.4 2.4 %collective-permute-done.51.refs_3_ = f32[2,16,512]{2,1,0:T(8,128)S(1)} collective-permute-done((f32[2,16,512]{2,1,0:T(8,128)S(1)}, f32[2,16,512]{2,1,0:T(8,128)S(1)}, u32[]{:S(2)}, u32[]{:S(2)}) %collective-permute-start.51) | collective-permute-done | bytes 65568 | tf_op jit(solution)/shard_map/ppermute | solution.py:74
  112.3 2.6 %collective-permute-start.53 = (f32[16,1280]{1,0:T(8,128)S(1)}, f32[16,1280]{1,0:T(8,128)S(1)}, u32[]{:S(2)}, u32[]{:S(2)}) collective-permute-start(f32[16,1280]{1,0:T(8,128)S(1)} %get-tuple-element.88), channel_id=1, source_target_pairs={{0,2},{1,3},{2,0},{3,1},{4,6},{5,7},{6,4},{7,5},{8,10},{9,11},{10,... | collective-permute-start | bytes 245768 | tf_op jit(solution)/shard_map/ppermute | solution.py:33
  114.9 1.7 %collective-permute-start.54 = (f32[16,1280]{1,0:T(8,128)S(1)}, f32[16,1280]{1,0:T(8,128)S(1)}, u32[]{:S(2)}, u32[]{:S(2)}) collective-permute-start(f32[16,1280]{1,0:T(8,128)S(1)} %get-tuple-element.89), channel_id=1, source_target_pairs={{0,3},{1,2},{2,1},{3,0},{4,7},{5,6},{6,5},{7,4},{8,11},{9,10},{10,... | collective-permute-start | bytes 245768 | tf_op jit(solution)/shard_map/ppermute | solution.py:33
  117.1 2.6 %collective-permute-done.53.refs_2_ = f32[16,1280]{1,0:T(8,128)S(1)} collective-permute-done((f32[16,1280]{1,0:T(8,128)S(1)}, f32[16,1280]{1,0:T(8,128)S(1)}, u32[]{:S(2)}, u32[]{:S(2)}) %collective-permute-start.53) | collective-permute-done | bytes 81952 | tf_op jit(solution)/shard_map/ppermute | solution.py:33
  119.8 1.5 %collective-permute-done.54.refs_3_ = f32[16,1280]{1,0:T(8,128)S(1)} collective-permute-done((f32[16,1280]{1,0:T(8,128)S(1)}, f32[16,1280]{1,0:T(8,128)S(1)}, u32[]{:S(2)}, u32[]{:S(2)}) %collective-permute-start.54) | collective-permute-done | bytes 81952 | tf_op jit(solution)/shard_map/ppermute | solution.py:33
  121.6 0.9 collective-permute-start.55
  122.5 1.5 %collective-permute-start.56 = (f32[16,256]{1,0:T(8,128)S(1)}, f32[16,256]{1,0:T(8,128)S(1)}, u32[]{:S(2)}, u32[]{:S(2)}) collective-permute-start(f32[16,256]{1,0:T(8,128)S(1)} %get-tuple-element.92.refs_0_.refs_6_), channel_id=1, source_target_pairs={{0,2},{1,3},{2,0},{3,1},{4,6},{5,7},{6,4},{7,5},{8,10},{9,11},{10,... | collective-permute-start | bytes 49160 | tf_op jit(solution)/shard_map/ppermute | solution.py:33
  124.0 2.1 %collective-permute-start.57 = (f32[16,256]{1,0:T(8,128)S(1)}, f32[16,256]{1,0:T(8,128)S(1)}, u32[]{:S(2)}, u32[]{:S(2)}) collective-permute-start(f32[16,256]{1,0:T(8,128)S(1)} %get-tuple-element.92.refs_0_.refs_6_), channel_id=1, source_target_pairs={{0,3},{1,2},{2,1},{3,0},{4,7},{5,6},{6,5},{7,4},{8,11},{9,10},{10,... | collective-permute-start | bytes 49160 | tf_op jit(solution)/shard_map/ppermute | solution.py:33
  126.0 1.1 collective-permute-done.56.refs_2_
  127.1 2.4 %collective-permute-done.57.refs_3_ = f32[16,256]{1,0:T(8,128)S(1)} collective-permute-done((f32[16,256]{1,0:T(8,128)S(1)}, f32[16,256]{1,0:T(8,128)S(1)}, u32[]{:S(2)}, u32[]{:S(2)}) %collective-permute-start.57) | collective-permute-done | bytes 16416 | tf_op jit(solution)/shard_map/ppermute | solution.py:33
  129.9 2.8 %collective-permute-start.59 = (f32[16,256]{1,0:T(8,128)S(1)}, f32[16,256]{1,0:T(8,128)S(1)}, u32[]{:S(2)}, u32[]{:S(2)}) collective-permute-start(f32[16,256]{1,0:T(8,128)S(1)} %shard_map.124.refs_0_), channel_id=1, source_target_pairs={{0,2},{1,3},{2,0},{3,1},{4,6},{5,7},{6,4},{7,5},{8,10},{9,11},{10,... | collective-permute-start | bytes 49160 | tf_op jit(solution)/shard_map/ppermute | solution.py:33
  132.6 1.6 %collective-permute-start.60 = (f32[16,256]{1,0:T(8,128)S(1)}, f32[16,256]{1,0:T(8,128)S(1)}, u32[]{:S(2)}, u32[]{:S(2)}) collective-permute-start(f32[16,256]{1,0:T(8,128)S(1)} %shard_map.124.refs_0_), channel_id=1, source_target_pairs={{0,3},{1,2},{2,1},{3,0},{4,7},{5,6},{6,5},{7,4},{8,11},{9,10},{10,... | collective-permute-start | bytes 49160 | tf_op jit(solution)/shard_map/ppermute | solution.py:33
  134.6 3.6 %collective-permute-done.60.refs_3_ = f32[16,256]{1,0:T(8,128)S(1)} collective-permute-done((f32[16,256]{1,0:T(8,128)S(1)}, f32[16,256]{1,0:T(8,128)S(1)}, u32[]{:S(2)}, u32[]{:S(2)}) %collective-permute-start.60) | collective-permute-done | bytes 16416 | tf_op jit(solution)/shard_map/ppermute | solution.py:33
  138.2 1.0 shard_map.125
  (162 shorter events, 11.6 us)
Async XLA Ops:
  1.9 10.1 %collective-permute-start = (f32[64,256]{1,0:T(8,128)S(1)}, f32[64,256]{1,0:T(8,128)S(1)}, u32[]{:S(2)}, u32[]{:S(2)}) collective-permute-start(f32[64,256]{1,0:T(8,128)S(1)} %get-tuple-element.49.refs_0_), channel_id=1, source_target_pairs={{0,1},{1,0},{2,3},{3,2},{4,5},{5,4},{6,7},{7,6},{8,9},{9,8},{10,11... | collective-permute-start | bytes 196616 | tf_op jit(solution)/shard_map/ppermute | solution.py:33
  5.0 10.5 %collective-permute-start.1 = (f32[64,256]{1,0:T(8,128)S(1)}, f32[64,256]{1,0:T(8,128)S(1)}, u32[]{:S(2)}, u32[]{:S(2)}) collective-permute-start(f32[64,256]{1,0:T(8,128)S(1)} %get-tuple-element.49.refs_0_), channel_id=1, source_target_pairs={{0,2},{1,3},{2,0},{3,1},{4,6},{5,7},{6,4},{7,5},{8,10},{9,11},{10,... | collective-permute-start | bytes 196616 | tf_op jit(solution)/shard_map/ppermute | solution.py:33
  7.6 7.9 %collective-permute-start.2 = (f32[64,256]{1,0:T(8,128)S(1)}, f32[64,256]{1,0:T(8,128)S(1)}, u32[]{:S(2)}, u32[]{:S(2)}) collective-permute-start(f32[64,256]{1,0:T(8,128)S(1)} %get-tuple-element.49.refs_0_), channel_id=1, source_target_pairs={{0,3},{1,2},{2,1},{3,0},{4,7},{5,6},{6,5},{7,4},{8,11},{9,10},{10,... | collective-permute-start | bytes 196616 | tf_op jit(solution)/shard_map/ppermute | solution.py:33
  7.6 12.8 %collective-permute-start.3 = (f32[64,256]{1,0:T(8,128)S(1)}, f32[64,256]{1,0:T(8,128)S(1)}, u32[]{:S(2)}, u32[]{:S(2)}) collective-permute-start(f32[64,256]{1,0:T(8,128)S(1)} %get-tuple-element.50.refs_0_), channel_id=1, source_target_pairs={{0,1},{1,0},{2,3},{3,2},{4,5},{5,4},{6,7},{7,6},{8,9},{9,8},{10,11... | collective-permute-start | bytes 196616 | tf_op jit(solution)/shard_map/ppermute | solution.py:33
  8.5 12.7 %collective-permute-start.4 = (f32[64,256]{1,0:T(8,128)S(1)}, f32[64,256]{1,0:T(8,128)S(1)}, u32[]{:S(2)}, u32[]{:S(2)}) collective-permute-start(f32[64,256]{1,0:T(8,128)S(1)} %get-tuple-element.50.refs_0_), channel_id=1, source_target_pairs={{0,2},{1,3},{2,0},{3,1},{4,6},{5,7},{6,4},{7,5},{8,10},{9,11},{10,... | collective-permute-start | bytes 196616 | tf_op jit(solution)/shard_map/ppermute | solution.py:33
  12.0 9.2 %collective-permute-start.5 = (f32[64,256]{1,0:T(8,128)S(1)}, f32[64,256]{1,0:T(8,128)S(1)}, u32[]{:S(2)}, u32[]{:S(2)}) collective-permute-start(f32[64,256]{1,0:T(8,128)S(1)} %get-tuple-element.50.refs_0_), channel_id=1, source_target_pairs={{0,3},{1,2},{2,1},{3,0},{4,7},{5,6},{6,5},{7,4},{8,11},{9,10},{10,... | collective-permute-start | bytes 196616 | tf_op jit(solution)/shard_map/ppermute | solution.py:33
  16.0 9.0 %collective-permute-start.6 = (f32[64,256]{1,0:T(8,128)S(1)}, f32[64,256]{1,0:T(8,128)S(1)}, u32[]{:S(2)}, u32[]{:S(2)}) collective-permute-start(f32[64,256]{1,0:T(8,128)S(1)} %shard_map.114.refs_0_), channel_id=1, source_target_pairs={{0,1},{1,0},{2,3},{3,2},{4,5},{5,4},{6,7},{7,6},{8,9},{9,8},{10,11... | collective-permute-start | bytes 196616 | tf_op jit(solution)/shard_map/ppermute | solution.py:33
  17.8 9.3 %collective-permute-start.7 = (f32[64,256]{1,0:T(8,128)S(1)}, f32[64,256]{1,0:T(8,128)S(1)}, u32[]{:S(2)}, u32[]{:S(2)}) collective-permute-start(f32[64,256]{1,0:T(8,128)S(1)} %shard_map.114.refs_0_), channel_id=1, source_target_pairs={{0,2},{1,3},{2,0},{3,1},{4,6},{5,7},{6,4},{7,5},{8,10},{9,11},{10,... | collective-permute-start | bytes 196616 | tf_op jit(solution)/shard_map/ppermute | solution.py:33
  20.4 6.8 %collective-permute-start.8 = (f32[64,256]{1,0:T(8,128)S(1)}, f32[64,256]{1,0:T(8,128)S(1)}, u32[]{:S(2)}, u32[]{:S(2)}) collective-permute-start(f32[64,256]{1,0:T(8,128)S(1)} %shard_map.114.refs_0_), channel_id=1, source_target_pairs={{0,3},{1,2},{2,1},{3,0},{4,7},{5,6},{6,5},{7,4},{8,11},{9,10},{10,... | collective-permute-start | bytes 196616 | tf_op jit(solution)/shard_map/ppermute | solution.py:33
  21.7 18.8 %copy-start.8 = (f32[1,4,256,1024]{3,2,1,0:T(8,128)S(1)}, f32[1,4,256,1024]{3,2,1,0:T(8,128)}, u32[]{:S(2)}) copy-start(f32[1,4,256,1024]{3,2,1,0:T(8,128)} %param.11) | copy-start | bytes 12582916
  21.7 13.4 %collective-permute-start.11 = (f32[64,256]{1,0:T(8,128)S(1)}, f32[64,256]{1,0:T(8,128)S(1)}, u32[]{:S(2)}, u32[]{:S(2)}) collective-permute-start(f32[64,256]{1,0:T(8,128)S(1)} %shard_map.115.refs_1_), channel_id=1, source_target_pairs={{0,2},{1,3},{2,0},{3,1},{4,6},{5,7},{6,4},{7,5},{8,10},{9,11},{10,... | collective-permute-start | bytes 196616 | tf_op jit(solution)/shard_map/ppermute | solution.py:33
  23.8 11.4 %collective-permute-start.12 = (f32[64,256]{1,0:T(8,128)S(1)}, f32[64,256]{1,0:T(8,128)S(1)}, u32[]{:S(2)}, u32[]{:S(2)}) collective-permute-start(f32[64,256]{1,0:T(8,128)S(1)} %shard_map.115.refs_1_), channel_id=1, source_target_pairs={{0,3},{1,2},{2,1},{3,0},{4,7},{5,6},{6,5},{7,4},{8,11},{9,10},{10,... | collective-permute-start | bytes 196616 | tf_op jit(solution)/shard_map/ppermute | solution.py:33
  25.0 10.1 %collective-permute-start.9 = (f32[64,256]{1,0:T(8,128)S(1)}, f32[64,256]{1,0:T(8,128)S(1)}, u32[]{:S(2)}, u32[]{:S(2)}) collective-permute-start(f32[64,256]{1,0:T(8,128)S(1)} %shard_map.115.refs_1_), channel_id=1, source_target_pairs={{0,1},{1,0},{2,3},{3,2},{4,5},{5,4},{6,7},{7,6},{8,9},{9,8},{10,11... | collective-permute-start | bytes 196616 | tf_op jit(solution)/shard_map/ppermute | solution.py:33
  28.0 12.5 %collective-permute-start.13 = (f32[64,256]{1,0:T(8,128)S(1)}, f32[64,256]{1,0:T(8,128)S(1)}, u32[]{:S(2)}, u32[]{:S(2)}) collective-permute-start(f32[64,256]{1,0:T(8,128)S(1)} %get-tuple-element.54), channel_id=1, source_target_pairs={{0,2},{1,3},{2,0},{3,1},{4,6},{5,7},{6,4},{7,5},{8,10},{9,11},{10,... | collective-permute-start | bytes 196616 | tf_op jit(solution)/shard_map/ppermute | solution.py:33
  33.3 7.2 %collective-permute-start.14 = (f32[64,256]{1,0:T(8,128)S(1)}, f32[64,256]{1,0:T(8,128)S(1)}, u32[]{:S(2)}, u32[]{:S(2)}) collective-permute-start(f32[64,256]{1,0:T(8,128)S(1)} %get-tuple-element.54), channel_id=1, source_target_pairs={{0,3},{1,2},{2,1},{3,0},{4,7},{5,6},{6,5},{7,4},{8,11},{9,10},{10,... | collective-permute-start | bytes 196616 | tf_op jit(solution)/shard_map/ppermute | solution.py:33
  35.1 5.3 %collective-permute-start.10 = (f32[64,256]{1,0:T(8,128)S(1)}, f32[64,256]{1,0:T(8,128)S(1)}, u32[]{:S(2)}, u32[]{:S(2)}) collective-permute-start(f32[64,256]{1,0:T(8,128)S(1)} %get-tuple-element.54), channel_id=1, source_target_pairs={{0,1},{1,0},{2,3},{3,2},{4,5},{5,4},{6,7},{7,6},{8,9},{9,8},{10,11... | collective-permute-start | bytes 196616 | tf_op jit(solution)/shard_map/ppermute | solution.py:33
  35.8 10.1 %collective-permute-start.16 = (f32[64,256]{1,0:T(8,128)S(1)}, f32[64,256]{1,0:T(8,128)S(1)}, u32[]{:S(2)}, u32[]{:S(2)}) collective-permute-start(f32[64,256]{1,0:T(8,128)S(1)} %get-tuple-element.56), channel_id=1, source_target_pairs={{0,2},{1,3},{2,0},{3,1},{4,6},{5,7},{6,4},{7,5},{8,10},{9,11},{10,... | collective-permute-start | bytes 196616 | tf_op jit(solution)/shard_map/ppermute | solution.py:33
  38.5 7.5 %collective-permute-start.17 = (f32[64,256]{1,0:T(8,128)S(1)}, f32[64,256]{1,0:T(8,128)S(1)}, u32[]{:S(2)}, u32[]{:S(2)}) collective-permute-start(f32[64,256]{1,0:T(8,128)S(1)} %get-tuple-element.56), channel_id=1, source_target_pairs={{0,3},{1,2},{2,1},{3,0},{4,7},{5,6},{6,5},{7,4},{8,11},{9,10},{10,... | collective-permute-start | bytes 196616 | tf_op jit(solution)/shard_map/ppermute | solution.py:33
  40.4 5.2 %collective-permute-start.15 = (f32[64,256]{1,0:T(8,128)S(1)}, f32[64,256]{1,0:T(8,128)S(1)}, u32[]{:S(2)}, u32[]{:S(2)}) collective-permute-start(f32[64,256]{1,0:T(8,128)S(1)} %get-tuple-element.56), channel_id=1, source_target_pairs={{0,1},{1,0},{2,3},{3,2},{4,5},{5,4},{6,7},{7,6},{8,9},{9,8},{10,11... | collective-permute-start | bytes 196616 | tf_op jit(solution)/shard_map/ppermute | solution.py:33
  41.1 9.9 %collective-permute-start.19 = (f32[64,256]{1,0:T(8,128)S(1)}, f32[64,256]{1,0:T(8,128)S(1)}, u32[]{:S(2)}, u32[]{:S(2)}) collective-permute-start(f32[64,256]{1,0:T(8,128)S(1)} %get-tuple-element.58.refs_2_), channel_id=1, source_target_pairs={{0,2},{1,3},{2,0},{3,1},{4,6},{5,7},{6,4},{7,5},{8,10},{9,11},{10,... | collective-permute-start | bytes 196616 | tf_op jit(solution)/shard_map/ppermute | solution.py:33
  43.8 7.3 %collective-permute-start.20 = (f32[64,256]{1,0:T(8,128)S(1)}, f32[64,256]{1,0:T(8,128)S(1)}, u32[]{:S(2)}, u32[]{:S(2)}) collective-permute-start(f32[64,256]{1,0:T(8,128)S(1)} %get-tuple-element.58.refs_2_), channel_id=1, source_target_pairs={{0,3},{1,2},{2,1},{3,0},{4,7},{5,6},{6,5},{7,4},{8,11},{9,10},{10,... | collective-permute-start | bytes 196616 | tf_op jit(solution)/shard_map/ppermute | solution.py:33
  45.6 5.4 %collective-permute-start.18 = (f32[64,256]{1,0:T(8,128)S(1)}, f32[64,256]{1,0:T(8,128)S(1)}, u32[]{:S(2)}, u32[]{:S(2)}) collective-permute-start(f32[64,256]{1,0:T(8,128)S(1)} %get-tuple-element.58.refs_2_), channel_id=1, source_target_pairs={{0,1},{1,0},{2,3},{3,2},{4,5},{5,4},{6,7},{7,6},{8,9},{9,8},{10,11... | collective-permute-start | bytes 196616 | tf_op jit(solution)/shard_map/ppermute | solution.py:33
  46.6 10.2 %collective-permute-start.23 = (f32[64,256]{1,0:T(8,128)S(1)}, f32[64,256]{1,0:T(8,128)S(1)}, u32[]{:S(2)}, u32[]{:S(2)}) collective-permute-start(f32[64,256]{1,0:T(8,128)S(1)} %get-tuple-element.60.refs_3_), channel_id=1, source_target_pairs={{0,2},{1,3},{2,0},{3,1},{4,6},{5,7},{6,4},{7,5},{8,10},{9,11},{10,... | collective-permute-start | bytes 196616 | tf_op jit(solution)/shard_map/ppermute | solution.py:33
  49.9 7.0 %collective-permute-start.24 = (f32[64,256]{1,0:T(8,128)S(1)}, f32[64,256]{1,0:T(8,128)S(1)}, u32[]{:S(2)}, u32[]{:S(2)}) collective-permute-start(f32[64,256]{1,0:T(8,128)S(1)} %get-tuple-element.60.refs_3_), channel_id=1, source_target_pairs={{0,3},{1,2},{2,1},{3,0},{4,7},{5,6},{6,5},{7,4},{8,11},{9,10},{10,... | collective-permute-start | bytes 196616 | tf_op jit(solution)/shard_map/ppermute | solution.py:33
  51.0 5.9 %collective-permute-start.21 = (f32[64,256]{1,0:T(8,128)S(1)}, f32[64,256]{1,0:T(8,128)S(1)}, u32[]{:S(2)}, u32[]{:S(2)}) collective-permute-start(f32[64,256]{1,0:T(8,128)S(1)} %get-tuple-element.60.refs_3_), channel_id=1, source_target_pairs={{0,1},{1,0},{2,3},{3,2},{4,5},{5,4},{6,7},{7,6},{8,9},{9,8},{10,11... | collective-permute-start | bytes 196616 | tf_op jit(solution)/shard_map/ppermute | solution.py:33
  51.8 10.5 %collective-permute-start.25 = (f32[64,256]{1,0:T(8,128)S(1)}, f32[64,256]{1,0:T(8,128)S(1)}, u32[]{:S(2)}, u32[]{:S(2)}) collective-permute-start(f32[64,256]{1,0:T(8,128)S(1)} %get-tuple-element.62), channel_id=1, source_target_pairs={{0,2},{1,3},{2,0},{3,1},{4,6},{5,7},{6,4},{7,5},{8,10},{9,11},{10,... | collective-permute-start | bytes 196616 | tf_op jit(solution)/shard_map/ppermute | solution.py:33
  55.0 7.2 %collective-permute-start.26 = (f32[64,256]{1,0:T(8,128)S(1)}, f32[64,256]{1,0:T(8,128)S(1)}, u32[]{:S(2)}, u32[]{:S(2)}) collective-permute-start(f32[64,256]{1,0:T(8,128)S(1)} %get-tuple-element.62), channel_id=1, source_target_pairs={{0,3},{1,2},{2,1},{3,0},{4,7},{5,6},{6,5},{7,4},{8,11},{9,10},{10,... | collective-permute-start | bytes 196616 | tf_op jit(solution)/shard_map/ppermute | solution.py:33
  56.8 5.4 %collective-permute-start.22 = (f32[64,256]{1,0:T(8,128)S(1)}, f32[64,256]{1,0:T(8,128)S(1)}, u32[]{:S(2)}, u32[]{:S(2)}) collective-permute-start(f32[64,256]{1,0:T(8,128)S(1)} %get-tuple-element.62), channel_id=1, source_target_pairs={{0,1},{1,0},{2,3},{3,2},{4,5},{5,4},{6,7},{7,6},{8,9},{9,8},{10,11... | collective-permute-start | bytes 196616 | tf_op jit(solution)/shard_map/ppermute | solution.py:33
  57.6 10.6 %collective-permute-start.28 = (f32[64,256]{1,0:T(8,128)S(1)}, f32[64,256]{1,0:T(8,128)S(1)}, u32[]{:S(2)}, u32[]{:S(2)}) collective-permute-start(f32[64,256]{1,0:T(8,128)S(1)} %get-tuple-element.64), channel_id=1, source_target_pairs={{0,2},{1,3},{2,0},{3,1},{4,6},{5,7},{6,4},{7,5},{8,10},{9,11},{10,... | collective-permute-start | bytes 196616 | tf_op jit(solution)/shard_map/ppermute | solution.py:33
  61.1 7.1 %collective-permute-start.29 = (f32[64,256]{1,0:T(8,128)S(1)}, f32[64,256]{1,0:T(8,128)S(1)}, u32[]{:S(2)}, u32[]{:S(2)}) collective-permute-start(f32[64,256]{1,0:T(8,128)S(1)} %get-tuple-element.64), channel_id=1, source_target_pairs={{0,3},{1,2},{2,1},{3,0},{4,7},{5,6},{6,5},{7,4},{8,11},{9,10},{10,... | collective-permute-start | bytes 196616 | tf_op jit(solution)/shard_map/ppermute | solution.py:33
  62.2 5.9 %collective-permute-start.27 = (f32[64,256]{1,0:T(8,128)S(1)}, f32[64,256]{1,0:T(8,128)S(1)}, u32[]{:S(2)}, u32[]{:S(2)}) collective-permute-start(f32[64,256]{1,0:T(8,128)S(1)} %get-tuple-element.64), channel_id=1, source_target_pairs={{0,1},{1,0},{2,3},{3,2},{4,5},{5,4},{6,7},{7,6},{8,9},{9,8},{10,11... | collective-permute-start | bytes 196616 | tf_op jit(solution)/shard_map/ppermute | solution.py:33
  62.9 10.6 %collective-permute-start.31 = (f32[64,256]{1,0:T(8,128)S(1)}, f32[64,256]{1,0:T(8,128)S(1)}, u32[]{:S(2)}, u32[]{:S(2)}) collective-permute-start(f32[64,256]{1,0:T(8,128)S(1)} %get-tuple-element.66.refs_4_), channel_id=1, source_target_pairs={{0,2},{1,3},{2,0},{3,1},{4,6},{5,7},{6,4},{7,5},{8,10},{9,11},{10,... | collective-permute-start | bytes 196616 | tf_op jit(solution)/shard_map/ppermute | solution.py:33
  66.3 7.3 %collective-permute-start.32 = (f32[64,256]{1,0:T(8,128)S(1)}, f32[64,256]{1,0:T(8,128)S(1)}, u32[]{:S(2)}, u32[]{:S(2)}) collective-permute-start(f32[64,256]{1,0:T(8,128)S(1)} %get-tuple-element.66.refs_4_), channel_id=1, source_target_pairs={{0,3},{1,2},{2,1},{3,0},{4,7},{5,6},{6,5},{7,4},{8,11},{9,10},{10,... | collective-permute-start | bytes 196616 | tf_op jit(solution)/shard_map/ppermute | solution.py:33
  68.1 5.3 %collective-permute-start.30 = (f32[64,256]{1,0:T(8,128)S(1)}, f32[64,256]{1,0:T(8,128)S(1)}, u32[]{:S(2)}, u32[]{:S(2)}) collective-permute-start(f32[64,256]{1,0:T(8,128)S(1)} %get-tuple-element.66.refs_4_), channel_id=1, source_target_pairs={{0,1},{1,0},{2,3},{3,2},{4,5},{5,4},{6,7},{7,6},{8,9},{9,8},{10,11... | collective-permute-start | bytes 196616 | tf_op jit(solution)/shard_map/ppermute | solution.py:33
  68.8 10.6 %collective-permute-start.35 = (f32[64,256]{1,0:T(8,128)S(1)}, f32[64,256]{1,0:T(8,128)S(1)}, u32[]{:S(2)}, u32[]{:S(2)}) collective-permute-start(f32[64,256]{1,0:T(8,128)S(1)} %get-tuple-element.68.refs_5_), channel_id=1, source_target_pairs={{0,2},{1,3},{2,0},{3,1},{4,6},{5,7},{6,4},{7,5},{8,10},{9,11},{10,... | collective-permute-start | bytes 196616 | tf_op jit(solution)/shard_map/ppermute | solution.py:33
  71.7 7.8 %collective-permute-start.36 = (f32[64,256]{1,0:T(8,128)S(1)}, f32[64,256]{1,0:T(8,128)S(1)}, u32[]{:S(2)}, u32[]{:S(2)}) collective-permute-start(f32[64,256]{1,0:T(8,128)S(1)} %get-tuple-element.68.refs_5_), channel_id=1, source_target_pairs={{0,3},{1,2},{2,1},{3,0},{4,7},{5,6},{6,5},{7,4},{8,11},{9,10},{10,... | collective-permute-start | bytes 196616 | tf_op jit(solution)/shard_map/ppermute | solution.py:33
  73.4 6.0 %collective-permute-start.33 = (f32[64,256]{1,0:T(8,128)S(1)}, f32[64,256]{1,0:T(8,128)S(1)}, u32[]{:S(2)}, u32[]{:S(2)}) collective-permute-start(f32[64,256]{1,0:T(8,128)S(1)} %get-tuple-element.68.refs_5_), channel_id=1, source_target_pairs={{0,1},{1,0},{2,3},{3,2},{4,5},{5,4},{6,7},{7,6},{8,9},{9,8},{10,11... | collective-permute-start | bytes 196616 | tf_op jit(solution)/shard_map/ppermute | solution.py:33
  74.2 10.6 %collective-permute-start.37 = (f32[64,256]{1,0:T(8,128)S(1)}, f32[64,256]{1,0:T(8,128)S(1)}, u32[]{:S(2)}, u32[]{:S(2)}) collective-permute-start(f32[64,256]{1,0:T(8,128)S(1)} %get-tuple-element.70), channel_id=1, source_target_pairs={{0,2},{1,3},{2,0},{3,1},{4,6},{5,7},{6,4},{7,5},{8,10},{9,11},{10,... | collective-permute-start | bytes 196616 | tf_op jit(solution)/shard_map/ppermute | solution.py:33
  77.9 6.9 %collective-permute-start.38 = (f32[64,256]{1,0:T(8,128)S(1)}, f32[64,256]{1,0:T(8,128)S(1)}, u32[]{:S(2)}, u32[]{:S(2)}) collective-permute-start(f32[64,256]{1,0:T(8,128)S(1)} %get-tuple-element.70), channel_id=1, source_target_pairs={{0,3},{1,2},{2,1},{3,0},{4,7},{5,6},{6,5},{7,4},{8,11},{9,10},{10,... | collective-permute-start | bytes 196616 | tf_op jit(solution)/shard_map/ppermute | solution.py:33
  79.4 5.2 %collective-permute-start.34 = (f32[64,256]{1,0:T(8,128)S(1)}, f32[64,256]{1,0:T(8,128)S(1)}, u32[]{:S(2)}, u32[]{:S(2)}) collective-permute-start(f32[64,256]{1,0:T(8,128)S(1)} %get-tuple-element.70), channel_id=1, source_target_pairs={{0,1},{1,0},{2,3},{3,2},{4,5},{5,4},{6,7},{7,6},{8,9},{9,8},{10,11... | collective-permute-start | bytes 196616 | tf_op jit(solution)/shard_map/ppermute | solution.py:33
  80.2 10.5 %collective-permute-start.40 = (f32[64,256]{1,0:T(8,128)S(1)}, f32[64,256]{1,0:T(8,128)S(1)}, u32[]{:S(2)}, u32[]{:S(2)}) collective-permute-start(f32[64,256]{1,0:T(8,128)S(1)} %get-tuple-element.72), channel_id=1, source_target_pairs={{0,2},{1,3},{2,0},{3,1},{4,6},{5,7},{6,4},{7,5},{8,10},{9,11},{10,... | collective-permute-start | bytes 196616 | tf_op jit(solution)/shard_map/ppermute | solution.py:33
  83.2 7.6 %collective-permute-start.41 = (f32[64,256]{1,0:T(8,128)S(1)}, f32[64,256]{1,0:T(8,128)S(1)}, u32[]{:S(2)}, u32[]{:S(2)}) collective-permute-start(f32[64,256]{1,0:T(8,128)S(1)} %get-tuple-element.72), channel_id=1, source_target_pairs={{0,3},{1,2},{2,1},{3,0},{4,7},{5,6},{6,5},{7,4},{8,11},{9,10},{10,... | collective-permute-start | bytes 196616 | tf_op jit(solution)/shard_map/ppermute | solution.py:33
  84.6 6.0 %collective-permute-start.39 = (f32[64,256]{1,0:T(8,128)S(1)}, f32[64,256]{1,0:T(8,128)S(1)}, u32[]{:S(2)}, u32[]{:S(2)}) collective-permute-start(f32[64,256]{1,0:T(8,128)S(1)} %get-tuple-element.72), channel_id=1, source_target_pairs={{0,1},{1,0},{2,3},{3,2},{4,5},{5,4},{6,7},{7,6},{8,9},{9,8},{10,11... | collective-permute-start | bytes 196616 | tf_op jit(solution)/shard_map/ppermute | solution.py:33
  85.6 10.3 %collective-permute-start.43 = (f32[64,256]{1,0:T(8,128)S(1)}, f32[64,256]{1,0:T(8,128)S(1)}, u32[]{:S(2)}, u32[]{:S(2)}) collective-permute-start(f32[64,256]{1,0:T(8,128)S(1)} %get-tuple-element.74.refs_6_), channel_id=1, source_target_pairs={{0,2},{1,3},{2,0},{3,1},{4,6},{5,7},{6,4},{7,5},{8,10},{9,11},{10,... | collective-permute-start | bytes 196616 | tf_op jit(solution)/shard_map/ppermute | solution.py:33
  88.5 7.3 %collective-permute-start.44 = (f32[64,256]{1,0:T(8,128)S(1)}, f32[64,256]{1,0:T(8,128)S(1)}, u32[]{:S(2)}, u32[]{:S(2)}) collective-permute-start(f32[64,256]{1,0:T(8,128)S(1)} %get-tuple-element.74.refs_6_), channel_id=1, source_target_pairs={{0,3},{1,2},{2,1},{3,0},{4,7},{5,6},{6,5},{7,4},{8,11},{9,10},{10,... | collective-permute-start | bytes 196616 | tf_op jit(solution)/shard_map/ppermute | solution.py:33
  90.7 5.2 %collective-permute-start.42 = (f32[64,256]{1,0:T(8,128)S(1)}, f32[64,256]{1,0:T(8,128)S(1)}, u32[]{:S(2)}, u32[]{:S(2)}) collective-permute-start(f32[64,256]{1,0:T(8,128)S(1)} %get-tuple-element.74.refs_6_), channel_id=1, source_target_pairs={{0,1},{1,0},{2,3},{3,2},{4,5},{5,4},{6,7},{7,6},{8,9},{9,8},{10,11... | collective-permute-start | bytes 196616 | tf_op jit(solution)/shard_map/ppermute | solution.py:33
  91.4 8.7 %collective-permute-start.46 = (f32[64,256]{1,0:T(8,128)S(1)}, f32[64,256]{1,0:T(8,128)S(1)}, u32[]{:S(2)}, u32[]{:S(2)}) collective-permute-start(f32[64,256]{1,0:T(8,128)S(1)} %get-tuple-element.76.refs_7_), channel_id=1, source_target_pairs={{0,2},{1,3},{2,0},{3,1},{4,6},{5,7},{6,4},{7,5},{8,10},{9,11},{10,... | collective-permute-start | bytes 196616 | tf_op jit(solution)/shard_map/ppermute | solution.py:33
  94.8 6.1 %collective-permute-start.47 = (f32[64,256]{1,0:T(8,128)S(1)}, f32[64,256]{1,0:T(8,128)S(1)}, u32[]{:S(2)}, u32[]{:S(2)}) collective-permute-start(f32[64,256]{1,0:T(8,128)S(1)} %get-tuple-element.76.refs_7_), channel_id=1, source_target_pairs={{0,3},{1,2},{2,1},{3,0},{4,7},{5,6},{6,5},{7,4},{8,11},{9,10},{10,... | collective-permute-start | bytes 196616 | tf_op jit(solution)/shard_map/ppermute | solution.py:33
  95.8 4.3 %collective-permute-start.45 = (f32[64,256]{1,0:T(8,128)S(1)}, f32[64,256]{1,0:T(8,128)S(1)}, u32[]{:S(2)}, u32[]{:S(2)}) collective-permute-start(f32[64,256]{1,0:T(8,128)S(1)} %get-tuple-element.76.refs_7_), channel_id=1, source_target_pairs={{0,1},{1,0},{2,3},{3,2},{4,5},{5,4},{6,7},{7,6},{8,9},{9,8},{10,11... | collective-permute-start | bytes 196616 | tf_op jit(solution)/shard_map/ppermute | solution.py:33
  96.0 20.7 %copy-start.3 = (f32[2,256,1024]{2,1,0:T(8,128)S(1)}, f32[2,256,1024]{2,1,0:T(8,128)}, u32[]{:S(2)}) copy-start(f32[2,256,1024]{2,1,0:T(8,128)} %refs_0_.1) | copy-start | bytes 6291460
  96.0 20.7 %copy-start.4 = (f32[1,256,1024]{2,1,0:T(8,128)S(1)}, f32[1,256,1024]{2,1,0:T(8,128)}, u32[]{:S(2)}) copy-start(f32[1,256,1024]{2,1,0:T(8,128)} %refs_1_.1) | copy-start | bytes 3145732
  102.1 1.4 %collective-permute-start.48 = (f32[4,16,512]{2,1,0:T(8,128)S(1)}, f32[4,16,512]{2,1,0:T(8,128)S(1)}, u32[]{:S(2)}, u32[]{:S(2)}) collective-permute-start(f32[4,16,512]{2,1,0:T(8,128)S(1)} %get-tuple-element.80), channel_id=1, source_target_pairs={{0,4},{4,0},{8,12},{12,8},{16,20},{20,16},{24,28},{28,24},{1,5},{5... | collective-permute-start | bytes 393224 | tf_op jit(solution)/shard_map/ppermute | solution.py:274
  103.5 4.6 %collective-permute-start.49 = (f32[2,16,512]{2,1,0:T(8,128)S(1)}, f32[2,16,512]{2,1,0:T(8,128)S(1)}, u32[]{:S(2)}, u32[]{:S(2)}) collective-permute-start(f32[2,16,512]{2,1,0:T(8,128)S(1)} %get-tuple-element.82), channel_id=1, source_target_pairs={{0,8},{4,12},{8,0},{12,4},{16,24},{20,28},{24,16},{28,20},{1,9},{5... | collective-permute-start | bytes 196616 | tf_op jit(solution)/shard_map/ppermute | solution.py:74
  105.1 4.3 %collective-permute-start.50 = (f32[2,16,512]{2,1,0:T(8,128)S(1)}, f32[2,16,512]{2,1,0:T(8,128)S(1)}, u32[]{:S(2)}, u32[]{:S(2)}) collective-permute-start(f32[2,16,512]{2,1,0:T(8,128)S(1)} %get-tuple-element.83), channel_id=1, source_target_pairs={{0,16},{4,20},{8,24},{12,28},{16,0},{20,4},{24,8},{28,12},{1,17},{... | collective-permute-start | bytes 196616 | tf_op jit(solution)/shard_map/ppermute | solution.py:74
  106.6 5.2 %collective-permute-start.51 = (f32[2,16,512]{2,1,0:T(8,128)S(1)}, f32[2,16,512]{2,1,0:T(8,128)S(1)}, u32[]{:S(2)}, u32[]{:S(2)}) collective-permute-start(f32[2,16,512]{2,1,0:T(8,128)S(1)} %get-tuple-element.84), channel_id=1, source_target_pairs={{0,24},{4,28},{8,16},{12,20},{16,8},{20,12},{24,0},{28,4},{1,25},{... | collective-permute-start | bytes 196616 | tf_op jit(solution)/shard_map/ppermute | solution.py:74
  112.2 4.9 %collective-permute-start.52 = (f32[16,1280]{1,0:T(8,128)S(1)}, f32[16,1280]{1,0:T(8,128)S(1)}, u32[]{:S(2)}, u32[]{:S(2)}) collective-permute-start(f32[16,1280]{1,0:T(8,128)S(1)} %get-tuple-element.87), channel_id=1, source_target_pairs={{0,1},{1,0},{2,3},{3,2},{4,5},{5,4},{6,7},{7,6},{8,9},{9,8},{10,11... | collective-permute-start | bytes 245768 | tf_op jit(solution)/shard_map/ppermute | solution.py:33
  112.3 7.5 %collective-permute-start.53 = (f32[16,1280]{1,0:T(8,128)S(1)}, f32[16,1280]{1,0:T(8,128)S(1)}, u32[]{:S(2)}, u32[]{:S(2)}) collective-permute-start(f32[16,1280]{1,0:T(8,128)S(1)} %get-tuple-element.88), channel_id=1, source_target_pairs={{0,2},{1,3},{2,0},{3,1},{4,6},{5,7},{6,4},{7,5},{8,10},{9,11},{10,... | collective-permute-start | bytes 245768 | tf_op jit(solution)/shard_map/ppermute | solution.py:33
  114.9 6.3 %collective-permute-start.54 = (f32[16,1280]{1,0:T(8,128)S(1)}, f32[16,1280]{1,0:T(8,128)S(1)}, u32[]{:S(2)}, u32[]{:S(2)}) collective-permute-start(f32[16,1280]{1,0:T(8,128)S(1)} %get-tuple-element.89), channel_id=1, source_target_pairs={{0,3},{1,2},{2,1},{3,0},{4,7},{5,6},{6,5},{7,4},{8,11},{9,10},{10,... | collective-permute-start | bytes 245768 | tf_op jit(solution)/shard_map/ppermute | solution.py:33
  121.6 4.4 %collective-permute-start.55 = (f32[16,256]{1,0:T(8,128)S(1)}, f32[16,256]{1,0:T(8,128)S(1)}, u32[]{:S(2)}, u32[]{:S(2)}) collective-permute-start(f32[16,256]{1,0:T(8,128)S(1)} %get-tuple-element.92.refs_0_.refs_6_), channel_id=1, source_target_pairs={{0,1},{1,0},{2,3},{3,2},{4,5},{5,4},{6,7},{7,6},{8,9},{9,8},{10,11... | collective-permute-start | bytes 49160 | tf_op jit(solution)/shard_map/ppermute | solution.py:33
  122.5 4.6 %collective-permute-start.56 = (f32[16,256]{1,0:T(8,128)S(1)}, f32[16,256]{1,0:T(8,128)S(1)}, u32[]{:S(2)}, u32[]{:S(2)}) collective-permute-start(f32[16,256]{1,0:T(8,128)S(1)} %get-tuple-element.92.refs_0_.refs_6_), channel_id=1, source_target_pairs={{0,2},{1,3},{2,0},{3,1},{4,6},{5,7},{6,4},{7,5},{8,10},{9,11},{10,... | collective-permute-start | bytes 49160 | tf_op jit(solution)/shard_map/ppermute | solution.py:33
  124.0 5.5 %collective-permute-start.57 = (f32[16,256]{1,0:T(8,128)S(1)}, f32[16,256]{1,0:T(8,128)S(1)}, u32[]{:S(2)}, u32[]{:S(2)}) collective-permute-start(f32[16,256]{1,0:T(8,128)S(1)} %get-tuple-element.92.refs_0_.refs_6_), channel_id=1, source_target_pairs={{0,3},{1,2},{2,1},{3,0},{4,7},{5,6},{6,5},{7,4},{8,11},{9,10},{10,... | collective-permute-start | bytes 49160 | tf_op jit(solution)/shard_map/ppermute | solution.py:33
  129.9 4.4 %collective-permute-start.58 = (f32[16,256]{1,0:T(8,128)S(1)}, f32[16,256]{1,0:T(8,128)S(1)}, u32[]{:S(2)}, u32[]{:S(2)}) collective-permute-start(f32[16,256]{1,0:T(8,128)S(1)} %shard_map.124.refs_0_), channel_id=1, source_target_pairs={{0,1},{1,0},{2,3},{3,2},{4,5},{5,4},{6,7},{7,6},{8,9},{9,8},{10,11... | collective-permute-start | bytes 49160 | tf_op jit(solution)/shard_map/ppermute | solution.py:33
  129.9 4.7 %collective-permute-start.59 = (f32[16,256]{1,0:T(8,128)S(1)}, f32[16,256]{1,0:T(8,128)S(1)}, u32[]{:S(2)}, u32[]{:S(2)}) collective-permute-start(f32[16,256]{1,0:T(8,128)S(1)} %shard_map.124.refs_0_), channel_id=1, source_target_pairs={{0,2},{1,3},{2,0},{3,1},{4,6},{5,7},{6,4},{7,5},{8,10},{9,11},{10,... | collective-permute-start | bytes 49160 | tf_op jit(solution)/shard_map/ppermute | solution.py:33
  132.6 5.5 %collective-permute-start.60 = (f32[16,256]{1,0:T(8,128)S(1)}, f32[16,256]{1,0:T(8,128)S(1)}, u32[]{:S(2)}, u32[]{:S(2)}) collective-permute-start(f32[16,256]{1,0:T(8,128)S(1)} %shard_map.124.refs_0_), channel_id=1, source_target_pairs={{0,3},{1,2},{2,1},{3,0},{4,7},{5,6},{6,5},{7,4},{8,11},{9,10},{10,... | collective-permute-start | bytes 49160 | tf_op jit(solution)/shard_map/ppermute | solution.py:33
  (7 other events, 78.0 us)

commit v18 on v17

--- a/solution.py
+++ b/solution.py
@@ -33,17 +33,32 @@
     return lax.ppermute(value, axis, pairs)
 
 
-def gather_rows(value, ties=()):
+def gather_rows(value, ties=(), swapped=False, far_first=False):
     members = lax.axis_size("grp")
     me = lax.axis_index("grp")
     rows = value.shape[1]
     pieces = [(me * rows, value)]
-    for distance in range(1, members):
+    distances = list(range(1, members))
+    if far_first:
+        distances = distances[1:] + distances[:1]
+    if swapped:
+        distances[1:3] = distances[2:0:-1]
+    for distance in distances:
         owner = partner(me, distance, members)
         tied = value
         if distance in dict(ties):
             tied = lax.optimization_barrier((value, dict(ties)[distance]))[0]
         pieces.append((owner * rows, send(tied, "grp", distance)))
+    return pieces
+
+
+def gather_far_first(value):
+    return [piece for _, piece in gather_rows(value, far_first=True)]
+
+
+def gather_sorted(pieces, swapped):
+    if swapped:
+        return pieces[:2] + pieces[3:1:-1] + pieces[4:]
     return pieces
 
 
@@ -196,11 +211,11 @@
     )
 
 
-def turn(rhs, first, last, streams):
+def turn(rhs, first, last, streams, after):
     rows, count = rhs.shape[2:]
     depth = count // streams
 
-    def body(rhs_ref, out, held, sem):
+    def body(rhs_ref, after_ref, out, held, sem):
         copy = pltpu.make_async_copy(rhs_ref.at[0, first:last], held, sem)
         copy.start()
         copy.wait()
@@ -212,8 +227,8 @@
     return local_kernel(
         body,
         [float_array(streams * (last - first), depth, rows)],
-        [rhs],
-        [ANY],
+        [rhs, after],
+        [ANY, ANY],
         scratch=[
             pltpu.VMEM((last - first, rows, count), jnp.float32),
             pltpu.SemaphoreType.DMA(()),
@@ -282,7 +297,7 @@
 
     portions = local_kernel(body, [float_array(inner, part, width)] * outer, held)
     return [portions[0]] + [
-        swap(portions[distance], "leaf", distance, inner) for distance in range(1, outer)
+        swap(portions[distance], "leaf", distance, inner) for distance in range(outer - 1, 0, -1)
     ]
 
 
@@ -388,7 +403,7 @@
         whole[:, j * width : (j + 1) * width] = value
 
 
-def apply_split(pieces, top, rest, index, base=None, begin=0, others=None):
+def apply_split(pieces, top, rest, index, base=None, begin=0, others=None, far_first=True):
     members = lax.axis_size("grp")
     part, width = pieces[0].shape
     rows, order = top.shape[1:]
@@ -397,7 +412,10 @@
     def body(*refs):
         top_ref, rest_ref = refs[members : members + 2]
         out, whole = refs[-2:]
-        put_in_order([refs[d][...] for d in range(members)], whole)
+        held = [refs[d][...] for d in range(members)]
+        if far_first:
+            held = held[:1] + held[-1:] + held[1:-1] if members > 2 else held
+        put_in_order(held, whole)
         result = split_product(whole[...], top_ref[index], rest_ref[index])
         if others is not None:
             for i in range(len(others)):
@@ -438,7 +456,6 @@
 
     streams = 2 if rhs_count % 16 == 0 else 1
     residuals = turn_first(rhs_local, streams)
-    later = turn(rhs_local, 1, supernodes, streams)
     first = diag_inv_local[0, 0]
     rounded = lax.reduce_precision(first, 8, 7)
     first_top = rounded.astype(jnp.bfloat16)[None]
@@ -452,12 +469,20 @@
         for i in range(streams):
             turn_taken = step > 0 and last is not None
             ties = [(1, last[0][1][1])] if step * streams + i > streams else []
-            pieces = gather_rows(values[i], ties)
-            if turn_taken and True:
+            pieces = gather_rows(values[i], ties, i % 2 == 1)
+            if step == 1 and i == 0:
+                later = turn(rhs_local, 1, supernodes, streams, pieces[1][1])
+            if turn_taken:
                 offset, piece = pieces[1]
                 pieces[1] = (offset, lax.optimization_barrier((piece, last[1]))[0])
             if step == 0:
-                owned = apply_split([p for _, p in pieces], first_top, first_rest, 0)
+                owned = apply_split(
+                    [p for _, p in gather_sorted(pieces, i % 2 == 1)],
+                    first_top,
+                    first_rest,
+                    0,
+                    far_first=False,
+                )
             else:
                 whole = assemble(pieces, order)
                 if step % 2 == 0:
@@ -479,7 +504,8 @@
     shares = share_out(
         received, jnp.swapaxes(rhs_anc, 1, 2), order, slots, tile_rows, tie
     )
-    payloads = [shares[0]] + [send(shares[d], "grp", d) for d in range(1, members)]
+    far_first = list(range(2, members)) + list(range(1, min(members, 2)))
+    payloads = [shares[0]] + [send(shares[d], "grp", d) for d in far_first]
     inverse_top, inverse_rest, below_top, below_rest = split_factors(
         [diag_inv_anc, sub_anc], shares[0]
     )
@@ -487,11 +513,11 @@
     solutions = [solution]
     ancestors = rhs_anc.shape[0]
     for ancestor in range(1, ancestors):
-        pieces = [piece for _, piece in gather_rows(solutions[-1])]
+        pieces = gather_far_first(solutions[-1])
         residual = apply_split(
             pieces, below_top, below_rest, ancestor - 1, left, (ancestor - 1) * rows
         )
-        pieces = [piece for _, piece in gather_rows(residual)]
+        pieces = gather_far_first(residual)
         others = solutions if ancestor + 1 == ancestors else None
         solved_now = apply_split(pieces, inverse_top, inverse_rest, ancestor, others=others)
         solutions.append(solved_now)

time: 139 us -> 138 us (level)
  starting transfers between devices: 95.6 us -> 94.2 us
    ppermute x57, waiting for transfers between devices: 17.1 us -> 19 us  [send(): return lax.ppermute(value, axis, pairs)]
  transfers between devices with their start and end apart: 61 -> 61, of which waited for: 14 -> 19; matrix products, arithmetic and copies ran while one was open for 7% -> 7% of each run, Pallas kernels for 3% -> 3%
where the time goes in v18:
time: 138 us
  starting transfers between devices  94.2 us (68%)
  waiting for transfers between devices  23 us (17%)
  matrix products  7.53 us (5%)
  Pallas kernels  7.52 us (5%)
  between operations  2.13 us (2%)
  local copies, waits for them, and re-layouts  1.82 us (1%)
  other arithmetic  1.41 us (1%)
    ppermute x57, starting transfers between devices, send(): return lax.ppermute(value, axis, pairs)  90.6 us
    ppermute x57, waiting for transfers between devices, send(): return lax.ppermute(value, axis, pairs)  19 us
    dot_general x12, matrix products, contract_last(): lax.dot_general(left, right, (((left.ndim - 1,), (right.ndim - 1,)), ((),...  7.53 us
    pallas_call x13, Pallas kernels, local_kernel(): pl.pallas_call(body, out_shape=list(outs), in_specs=specs or [VMEM] * len...  7.52 us
    ppermute x3, starting transfers between devices, swap(): return lax.ppermute(value, axis, pairs)  3.55 us
  transfers between devices with their start and end apart: 61, of which 19 were waited for; matrix products, arithmetic and copies ran while one was open for 7% of the time, Pallas kernels for 3%

profile of v18, /device:TPU:0, one launch (start us, length us, event | category | flops | bytes accessed | tf_op | source)
XLA Modules:
  0.0 137.7 jit_solution(10263348989050873002)
XLA Ops:
  0.6 1.0 copy-done.2
  1.9 3.1 %collective-permute-start = (f32[64,256]{1,0:T(8,128)S(1)}, f32[64,256]{1,0:T(8,128)S(1)}, u32[]{:S(2)}, u32[]{:S(2)}) collective-permute-start(f32[64,256]{1,0:T(8,128)S(1)} %get-tuple-element.49.refs_0_), channel_id=1, source_target_pairs={{0,1},{1,0},{2,3},{3,2},{4,5},{5,4},{6,7},{7,6},{8,9},{9,8},{10,11... | collective-permute-start | bytes 196616 | tf_op jit(solution)/shard_map/ppermute | solution.py:33
  5.0 2.6 %collective-permute-start.1 = (f32[64,256]{1,0:T(8,128)S(1)}, f32[64,256]{1,0:T(8,128)S(1)}, u32[]{:S(2)}, u32[]{:S(2)}) collective-permute-start(f32[64,256]{1,0:T(8,128)S(1)} %get-tuple-element.49.refs_0_), channel_id=1, source_target_pairs={{0,2},{1,3},{2,0},{3,1},{4,6},{5,7},{6,4},{7,5},{8,10},{9,11},{10,... | collective-permute-start | bytes 196616 | tf_op jit(solution)/shard_map/ppermute | solution.py:33
  7.6 0.9 collective-permute-start.3
  8.5 3.5 %collective-permute-start.4 = (f32[64,256]{1,0:T(8,128)S(1)}, f32[64,256]{1,0:T(8,128)S(1)}, u32[]{:S(2)}, u32[]{:S(2)}) collective-permute-start(f32[64,256]{1,0:T(8,128)S(1)} %get-tuple-element.50.refs_0_), channel_id=1, source_target_pairs={{0,2},{1,3},{2,0},{3,1},{4,6},{5,7},{6,4},{7,5},{8,10},{9,11},{10,... | collective-permute-start | bytes 196616 | tf_op jit(solution)/shard_map/ppermute | solution.py:33
  12.0 1.4 %fusion = (bf16[1,256,1024]{2,1,0:T(8,128)(2,1)S(1)}, bf16[1,256,1024]{2,1,0:T(8,128)(2,1)S(1)}) fusion(f32[1,4,256,1024]{3,2,1,0:T(8,128)} %param.11), kind=kLoop, calls=%fused_computation.2 | loop fusion | flops 1048576 | bytes 2097152 | tf_op jit(solution)/shard_map/convert_element_type | solution.py:462
  14.6 3.0 %collective-permute-start.6 = (f32[64,256]{1,0:T(8,128)S(1)}, f32[64,256]{1,0:T(8,128)S(1)}, u32[]{:S(2)}, u32[]{:S(2)}) collective-permute-start(f32[64,256]{1,0:T(8,128)S(1)} %shard_map.114.refs_0_), channel_id=1, source_target_pairs={{0,1},{1,0},{2,3},{3,2},{4,5},{5,4},{6,7},{7,6},{8,9},{9,8},{10,11... | collective-permute-start | bytes 196616 | tf_op jit(solution)/shard_map/ppermute | solution.py:33
  17.7 2.1 %collective-permute-start.7 = (f32[64,256]{1,0:T(8,128)S(1)}, f32[64,256]{1,0:T(8,128)S(1)}, u32[]{:S(2)}, u32[]{:S(2)}) collective-permute-start(f32[64,256]{1,0:T(8,128)S(1)} %shard_map.114.refs_0_), channel_id=1, source_target_pairs={{0,2},{1,3},{2,0},{3,1},{4,6},{5,7},{6,4},{7,5},{8,10},{9,11},{10,... | collective-permute-start | bytes 196616 | tf_op jit(solution)/shard_map/ppermute | solution.py:33
  19.8 1.4 %collective-permute-start.8 = (f32[64,256]{1,0:T(8,128)S(1)}, f32[64,256]{1,0:T(8,128)S(1)}, u32[]{:S(2)}, u32[]{:S(2)}) collective-permute-start(f32[64,256]{1,0:T(8,128)S(1)} %shard_map.114.refs_0_), channel_id=1, source_target_pairs={{0,3},{1,2},{2,1},{3,0},{4,7},{5,6},{6,5},{7,4},{8,11},{9,10},{10,... | collective-permute-start | bytes 196616 | tf_op jit(solution)/shard_map/ppermute | solution.py:33
  21.7 2.5 %collective-permute-start.11 = (f32[64,256]{1,0:T(8,128)S(1)}, f32[64,256]{1,0:T(8,128)S(1)}, u32[]{:S(2)}, u32[]{:S(2)}) collective-permute-start(f32[64,256]{1,0:T(8,128)S(1)} %shard_map.115.refs_1_), channel_id=1, source_target_pairs={{0,3},{1,2},{2,1},{3,0},{4,7},{5,6},{6,5},{7,4},{8,11},{9,10},{10,... | collective-permute-start | bytes 196616 | tf_op jit(solution)/shard_map/ppermute | solution.py:33
  24.3 2.0 %collective-permute-start.9 = (f32[64,256]{1,0:T(8,128)S(1)}, f32[64,256]{1,0:T(8,128)S(1)}, u32[]{:S(2)}, u32[]{:S(2)}) collective-permute-start(f32[64,256]{1,0:T(8,128)S(1)} %shard_map.115.refs_1_), channel_id=1, source_target_pairs={{0,1},{1,0},{2,3},{3,2},{4,5},{5,4},{6,7},{7,6},{8,9},{9,8},{10,11... | collective-permute-start | bytes 196616 | tf_op jit(solution)/shard_map/ppermute | solution.py:33
  27.4 6.1 %collective-permute-start.13 = (f32[64,256]{1,0:T(8,128)S(1)}, f32[64,256]{1,0:T(8,128)S(1)}, u32[]{:S(2)}, u32[]{:S(2)}) collective-permute-start(f32[64,256]{1,0:T(8,128)S(1)} %get-tuple-element.54), channel_id=1, source_target_pairs={{0,2},{1,3},{2,0},{3,1},{4,6},{5,7},{6,4},{7,5},{8,10},{9,11},{10,... | collective-permute-start | bytes 196616 | tf_op jit(solution)/shard_map/ppermute | solution.py:33
  34.3 0.6 constant_dynamic-update-slice_fusion.43
  34.9 3.2 %collective-permute-start.16 = (f32[64,256]{1,0:T(8,128)S(1)}, f32[64,256]{1,0:T(8,128)S(1)}, u32[]{:S(2)}, u32[]{:S(2)}) collective-permute-start(f32[64,256]{1,0:T(8,128)S(1)} %get-tuple-element.56), channel_id=1, source_target_pairs={{0,3},{1,2},{2,1},{3,0},{4,7},{5,6},{6,5},{7,4},{8,11},{9,10},{10,... | collective-permute-start | bytes 196616 | tf_op jit(solution)/shard_map/ppermute | solution.py:33
  38.1 0.6 collective-permute-start.17
  39.0 1.6 %collective-permute-start.15 = (f32[64,256]{1,0:T(8,128)S(1)}, f32[64,256]{1,0:T(8,128)S(1)}, u32[]{:S(2)}, u32[]{:S(2)}) collective-permute-start(f32[64,256]{1,0:T(8,128)S(1)} %get-tuple-element.56), channel_id=1, source_target_pairs={{0,1},{1,0},{2,3},{3,2},{4,5},{5,4},{6,7},{7,6},{8,9},{9,8},{10,11... | collective-permute-start | bytes 196616 | tf_op jit(solution)/shard_map/ppermute | solution.py:33
  41.4 4.3 %collective-permute-start.19 = (f32[64,256]{1,0:T(8,128)S(1)}, f32[64,256]{1,0:T(8,128)S(1)}, u32[]{:S(2)}, u32[]{:S(2)}) collective-permute-start(f32[64,256]{1,0:T(8,128)S(1)} %get-tuple-element.58.refs_2_), channel_id=1, source_target_pairs={{0,2},{1,3},{2,0},{3,1},{4,6},{5,7},{6,4},{7,5},{8,10},{9,11},{10,... | collective-permute-start | bytes 196616 | tf_op jit(solution)/shard_map/ppermute | solution.py:33
  45.7 0.6 collective-permute-start.18
  47.1 3.7 %collective-permute-start.23 = (f32[64,256]{1,0:T(8,128)S(1)}, f32[64,256]{1,0:T(8,128)S(1)}, u32[]{:S(2)}, u32[]{:S(2)}) collective-permute-start(f32[64,256]{1,0:T(8,128)S(1)} %get-tuple-element.60.refs_3_), channel_id=1, source_target_pairs={{0,3},{1,2},{2,1},{3,0},{4,7},{5,6},{6,5},{7,4},{8,11},{9,10},{10,... | collective-permute-start | bytes 196616 | tf_op jit(solution)/shard_map/ppermute | solution.py:33
  51.0 1.9 %collective-permute-start.21 = (f32[64,256]{1,0:T(8,128)S(1)}, f32[64,256]{1,0:T(8,128)S(1)}, u32[]{:S(2)}, u32[]{:S(2)}) collective-permute-start(f32[64,256]{1,0:T(8,128)S(1)} %get-tuple-element.60.refs_3_), channel_id=1, source_target_pairs={{0,1},{1,0},{2,3},{3,2},{4,5},{5,4},{6,7},{7,6},{8,9},{9,8},{10,11... | collective-permute-start | bytes 196616 | tf_op jit(solution)/shard_map/ppermute | solution.py:33
  53.6 4.8 %collective-permute-start.25 = (f32[64,256]{1,0:T(8,128)S(1)}, f32[64,256]{1,0:T(8,128)S(1)}, u32[]{:S(2)}, u32[]{:S(2)}) collective-permute-start(f32[64,256]{1,0:T(8,128)S(1)} %get-tuple-element.62), channel_id=1, source_target_pairs={{0,2},{1,3},{2,0},{3,1},{4,6},{5,7},{6,4},{7,5},{8,10},{9,11},{10,... | collective-permute-start | bytes 196616 | tf_op jit(solution)/shard_map/ppermute | solution.py:33
  58.4 0.6 collective-permute-start.22
  59.8 4.1 %collective-permute-start.28 = (f32[64,256]{1,0:T(8,128)S(1)}, f32[64,256]{1,0:T(8,128)S(1)}, u32[]{:S(2)}, u32[]{:S(2)}) collective-permute-start(f32[64,256]{1,0:T(8,128)S(1)} %get-tuple-element.64), channel_id=1, source_target_pairs={{0,3},{1,2},{2,1},{3,0},{4,7},{5,6},{6,5},{7,4},{8,11},{9,10},{10,... | collective-permute-start | bytes 196616 | tf_op jit(solution)/shard_map/ppermute | solution.py:33
  63.9 0.6 collective-permute-start.29
  65.7 4.1 %collective-permute-start.31 = (f32[64,256]{1,0:T(8,128)S(1)}, f32[64,256]{1,0:T(8,128)S(1)}, u32[]{:S(2)}, u32[]{:S(2)}) collective-permute-start(f32[64,256]{1,0:T(8,128)S(1)} %get-tuple-element.66.refs_4_), channel_id=1, source_target_pairs={{0,2},{1,3},{2,0},{3,1},{4,6},{5,7},{6,4},{7,5},{8,10},{9,11},{10,... | collective-permute-start | bytes 196616 | tf_op jit(solution)/shard_map/ppermute | solution.py:33
  69.8 0.6 collective-permute-start.30
  70.5 2.9 %collective-permute-done.29 = f32[64,256]{1,0:T(8,128)S(1)} collective-permute-done((f32[64,256]{1,0:T(8,128)S(1)}, f32[64,256]{1,0:T(8,128)S(1)}, u32[]{:S(2)}, u32[]{:S(2)}) %collective-permute-start.29) | collective-permute-done | bytes 65568 | tf_op jit(solution)/shard_map/ppermute | solution.py:33
  74.1 1.9 %collective-permute-start.35 = (f32[64,256]{1,0:T(8,128)S(1)}, f32[64,256]{1,0:T(8,128)S(1)}, u32[]{:S(2)}, u32[]{:S(2)}) collective-permute-start(f32[64,256]{1,0:T(8,128)S(1)} %get-tuple-element.68.refs_5_), channel_id=1, source_target_pairs={{0,3},{1,2},{2,1},{3,0},{4,7},{5,6},{6,5},{7,4},{8,11},{9,10},{10,... | collective-permute-start | bytes 196616 | tf_op jit(solution)/shard_map/ppermute | solution.py:33
  75.9 2.6 %collective-permute-start.33 = (f32[64,256]{1,0:T(8,128)S(1)}, f32[64,256]{1,0:T(8,128)S(1)}, u32[]{:S(2)}, u32[]{:S(2)}) collective-permute-start(f32[64,256]{1,0:T(8,128)S(1)} %get-tuple-element.68.refs_5_), channel_id=1, source_target_pairs={{0,1},{1,0},{2,3},{3,2},{4,5},{5,4},{6,7},{7,6},{8,9},{9,8},{10,11... | collective-permute-start | bytes 196616 | tf_op jit(solution)/shard_map/ppermute | solution.py:33
  79.8 2.1 %collective-permute-start.38 = (f32[64,256]{1,0:T(8,128)S(1)}, f32[64,256]{1,0:T(8,128)S(1)}, u32[]{:S(2)}, u32[]{:S(2)}) collective-permute-start(f32[64,256]{1,0:T(8,128)S(1)} %get-tuple-element.70), channel_id=1, source_target_pairs={{0,3},{1,2},{2,1},{3,0},{4,7},{5,6},{6,5},{7,4},{8,11},{9,10},{10,... | collective-permute-start | bytes 196616 | tf_op jit(solution)/shard_map/ppermute | solution.py:33
  81.9 1.6 %collective-permute-start.34 = (f32[64,256]{1,0:T(8,128)S(1)}, f32[64,256]{1,0:T(8,128)S(1)}, u32[]{:S(2)}, u32[]{:S(2)}) collective-permute-start(f32[64,256]{1,0:T(8,128)S(1)} %get-tuple-element.70), channel_id=1, source_target_pairs={{0,1},{1,0},{2,3},{3,2},{4,5},{5,4},{6,7},{7,6},{8,9},{9,8},{10,11... | collective-permute-start | bytes 196616 | tf_op jit(solution)/shard_map/ppermute | solution.py:33
  83.5 0.9 collective-permute-done.36
  84.5 0.6 constant_dynamic-update-slice_fusion.11
  85.1 2.9 %collective-permute-start.40 = (f32[64,256]{1,0:T(8,128)S(1)}, f32[64,256]{1,0:T(8,128)S(1)}, u32[]{:S(2)}, u32[]{:S(2)}) collective-permute-start(f32[64,256]{1,0:T(8,128)S(1)} %get-tuple-element.72), channel_id=1, source_target_pairs={{0,3},{1,2},{2,1},{3,0},{4,7},{5,6},{6,5},{7,4},{8,11},{9,10},{10,... | collective-permute-start | bytes 196616 | tf_op jit(solution)/shard_map/ppermute | solution.py:33
  88.0 1.5 %collective-permute-start.39 = (f32[64,256]{1,0:T(8,128)S(1)}, f32[64,256]{1,0:T(8,128)S(1)}, u32[]{:S(2)}, u32[]{:S(2)}) collective-permute-start(f32[64,256]{1,0:T(8,128)S(1)} %get-tuple-element.72), channel_id=1, source_target_pairs={{0,1},{1,0},{2,3},{3,2},{4,5},{5,4},{6,7},{7,6},{8,9},{9,8},{10,11... | collective-permute-start | bytes 196616 | tf_op jit(solution)/shard_map/ppermute | solution.py:33
  90.3 1.5 %collective-permute-start.43 = (f32[64,256]{1,0:T(8,128)S(1)}, f32[64,256]{1,0:T(8,128)S(1)}, u32[]{:S(2)}, u32[]{:S(2)}) collective-permute-start(f32[64,256]{1,0:T(8,128)S(1)} %get-tuple-element.74.refs_6_), channel_id=1, source_target_pairs={{0,2},{1,3},{2,0},{3,1},{4,6},{5,7},{6,4},{7,5},{8,10},{9,11},{10,... | collective-permute-start | bytes 196616 | tf_op jit(solution)/shard_map/ppermute | solution.py:33
  91.7 1.5 %collective-permute-start.44 = (f32[64,256]{1,0:T(8,128)S(1)}, f32[64,256]{1,0:T(8,128)S(1)}, u32[]{:S(2)}, u32[]{:S(2)}) collective-permute-start(f32[64,256]{1,0:T(8,128)S(1)} %get-tuple-element.74.refs_6_), channel_id=1, source_target_pairs={{0,3},{1,2},{2,1},{3,0},{4,7},{5,6},{6,5},{7,4},{8,11},{9,10},{10,... | collective-permute-start | bytes 196616 | tf_op jit(solution)/shard_map/ppermute | solution.py:33
  94.9 2.5 %collective-permute-start.46 = (f32[64,256]{1,0:T(8,128)S(1)}, f32[64,256]{1,0:T(8,128)S(1)}, u32[]{:S(2)}, u32[]{:S(2)}) collective-permute-start(f32[64,256]{1,0:T(8,128)S(1)} %get-tuple-element.76.refs_7_), channel_id=1, source_target_pairs={{0,3},{1,2},{2,1},{3,0},{4,7},{5,6},{6,5},{7,4},{8,11},{9,10},{10,... | collective-permute-start | bytes 196616 | tf_op jit(solution)/shard_map/ppermute | solution.py:33
  97.9 0.7 collective-permute-done.42
  98.6 0.8 collective-permute-start.45
  99.5 1.2 shard_map.117.refs_0_
  100.7 2.8 %collective-permute-done.45 = f32[64,256]{1,0:T(8,128)S(1)} collective-permute-done((f32[64,256]{1,0:T(8,128)S(1)}, f32[64,256]{1,0:T(8,128)S(1)}, u32[]{:S(2)}, u32[]{:S(2)}) %collective-permute-start.45) | collective-permute-done | bytes 65568 | tf_op jit(solution)/shard_map/ppermute | solution.py:33
  103.6 1.2 shard_map.118
  104.9 1.3 collective-permute-done.48.refs_1_
  106.2 2.2 %collective-permute-start.49 = (f32[2,16,512]{2,1,0:T(8,128)S(1)}, f32[2,16,512]{2,1,0:T(8,128)S(1)}, u32[]{:S(2)}, u32[]{:S(2)}) collective-permute-start(f32[2,16,512]{2,1,0:T(8,128)S(1)} %get-tuple-element.82), channel_id=1, source_target_pairs={{0,24},{4,28},{8,16},{12,20},{16,8},{20,12},{24,0},{28,4},{1,25},{... | collective-permute-start | bytes 196616 | tf_op jit(solution)/shard_map/ppermute | solution.py:89
  108.4 0.8 collective-permute-start.50
  109.8 1.0 shard_map.119
  110.8 0.7 collective-permute-done.49.refs_1_
  111.5 1.3 collective-permute-done.50.refs_2_
  112.8 0.7 collective-permute-done.51.refs_3_
  113.9 1.2 collective-permute-start.52
  115.2 1.3 collective-permute-start.53
  116.5 1.0 collective-permute-start.54
  117.9 3.9 %collective-permute-done.52.refs_1_ = f32[16,1280]{1,0:T(8,128)S(1)} collective-permute-done((f32[16,1280]{1,0:T(8,128)S(1)}, f32[16,1280]{1,0:T(8,128)S(1)}, u32[]{:S(2)}, u32[]{:S(2)}) %collective-permute-start.52) | collective-permute-done | bytes 81952 | tf_op jit(solution)/shard_map/ppermute | solution.py:33
  121.8 0.7 collective-permute-done.54.refs_3_
  122.9 1.2 collective-permute-start.55
  124.1 1.9 %collective-permute-start.56 = (f32[16,256]{1,0:T(8,128)S(1)}, f32[16,256]{1,0:T(8,128)S(1)}, u32[]{:S(2)}, u32[]{:S(2)}) collective-permute-start(f32[16,256]{1,0:T(8,128)S(1)} %get-tuple-element.92.refs_0_.refs_6_), channel_id=1, source_target_pairs={{0,3},{1,2},{2,1},{3,0},{4,7},{5,6},{6,5},{7,4},{8,11},{9,10},{10,... | collective-permute-start | bytes 49160 | tf_op jit(solution)/shard_map/ppermute | solution.py:33
  126.4 1.2 collective-permute-done.55.refs_1_
  127.6 2.1 %collective-permute-done.56.refs_2_ = f32[16,256]{1,0:T(8,128)S(1)} collective-permute-done((f32[16,256]{1,0:T(8,128)S(1)}, f32[16,256]{1,0:T(8,128)S(1)}, u32[]{:S(2)}, u32[]{:S(2)}) %collective-permute-start.56) | collective-permute-done | bytes 16416 | tf_op jit(solution)/shard_map/ppermute | solution.py:33
  130.8 2.1 %collective-permute-start.59 = (f32[16,256]{1,0:T(8,128)S(1)}, f32[16,256]{1,0:T(8,128)S(1)}, u32[]{:S(2)}, u32[]{:S(2)}) collective-permute-start(f32[16,256]{1,0:T(8,128)S(1)} %shard_map.124.refs_0_), channel_id=1, source_target_pairs={{0,3},{1,2},{2,1},{3,0},{4,7},{5,6},{6,5},{7,4},{8,11},{9,10},{10,... | collective-permute-start | bytes 49160 | tf_op jit(solution)/shard_map/ppermute | solution.py:33
  132.9 0.8 collective-permute-start.60
  133.7 1.1 collective-permute-done.58.refs_1_
  134.8 1.5 %collective-permute-done.59.refs_2_ = f32[16,256]{1,0:T(8,128)S(1)} collective-permute-done((f32[16,256]{1,0:T(8,128)S(1)}, f32[16,256]{1,0:T(8,128)S(1)}, u32[]{:S(2)}, u32[]{:S(2)}) %collective-permute-start.59) | collective-permute-done | bytes 16416 | tf_op jit(solution)/shard_map/ppermute | solution.py:33
  136.6 1.0 shard_map.125
  (162 shorter events, 16.1 us)
Async XLA Ops:
  1.7 24.6 %copy-start.3 = (f32[1,4,256,128]{3,2,1,0:T(8,128)S(1)}, f32[1,4,256,128]{3,2,1,0:T(8,128)}, u32[]{:S(2)}) copy-start(f32[1,4,256,128]{3,2,1,0:T(8,128)} %rhs_ref.3) | copy-start | bytes 1572868
  1.9 10.1 %collective-permute-start = (f32[64,256]{1,0:T(8,128)S(1)}, f32[64,256]{1,0:T(8,128)S(1)}, u32[]{:S(2)}, u32[]{:S(2)}) collective-permute-start(f32[64,256]{1,0:T(8,128)S(1)} %get-tuple-element.49.refs_0_), channel_id=1, source_target_pairs={{0,1},{1,0},{2,3},{3,2},{4,5},{5,4},{6,7},{7,6},{8,9},{9,8},{10,11... | collective-permute-start | bytes 196616 | tf_op jit(solution)/shard_map/ppermute | solution.py:33
  5.0 9.1 %collective-permute-start.1 = (f32[64,256]{1,0:T(8,128)S(1)}, f32[64,256]{1,0:T(8,128)S(1)}, u32[]{:S(2)}, u32[]{:S(2)}) collective-permute-start(f32[64,256]{1,0:T(8,128)S(1)} %get-tuple-element.49.refs_0_), channel_id=1, source_target_pairs={{0,2},{1,3},{2,0},{3,1},{4,6},{5,7},{6,4},{7,5},{8,10},{9,11},{10,... | collective-permute-start | bytes 196616 | tf_op jit(solution)/shard_map/ppermute | solution.py:33
  7.6 6.6 %collective-permute-start.2 = (f32[64,256]{1,0:T(8,128)S(1)}, f32[64,256]{1,0:T(8,128)S(1)}, u32[]{:S(2)}, u32[]{:S(2)}) collective-permute-start(f32[64,256]{1,0:T(8,128)S(1)} %get-tuple-element.49.refs_0_), channel_id=1, source_target_pairs={{0,3},{1,2},{2,1},{3,0},{4,7},{5,6},{6,5},{7,4},{8,11},{9,10},{10,... | collective-permute-start | bytes 196616 | tf_op jit(solution)/shard_map/ppermute | solution.py:33
  7.6 12.2 %collective-permute-start.3 = (f32[64,256]{1,0:T(8,128)S(1)}, f32[64,256]{1,0:T(8,128)S(1)}, u32[]{:S(2)}, u32[]{:S(2)}) collective-permute-start(f32[64,256]{1,0:T(8,128)S(1)} %get-tuple-element.50.refs_0_), channel_id=1, source_target_pairs={{0,1},{1,0},{2,3},{3,2},{4,5},{5,4},{6,7},{7,6},{8,9},{9,8},{10,11... | collective-permute-start | bytes 196616 | tf_op jit(solution)/shard_map/ppermute | solution.py:33
  8.5 12.7 %collective-permute-start.4 = (f32[64,256]{1,0:T(8,128)S(1)}, f32[64,256]{1,0:T(8,128)S(1)}, u32[]{:S(2)}, u32[]{:S(2)}) collective-permute-start(f32[64,256]{1,0:T(8,128)S(1)} %get-tuple-element.50.refs_0_), channel_id=1, source_target_pairs={{0,2},{1,3},{2,0},{3,1},{4,6},{5,7},{6,4},{7,5},{8,10},{9,11},{10,... | collective-permute-start | bytes 196616 | tf_op jit(solution)/shard_map/ppermute | solution.py:33
  12.0 9.2 %collective-permute-start.5 = (f32[64,256]{1,0:T(8,128)S(1)}, f32[64,256]{1,0:T(8,128)S(1)}, u32[]{:S(2)}, u32[]{:S(2)}) collective-permute-start(f32[64,256]{1,0:T(8,128)S(1)} %get-tuple-element.50.refs_0_), channel_id=1, source_target_pairs={{0,3},{1,2},{2,1},{3,0},{4,7},{5,6},{6,5},{7,4},{8,11},{9,10},{10,... | collective-permute-start | bytes 196616 | tf_op jit(solution)/shard_map/ppermute | solution.py:33
  14.6 9.6 %collective-permute-start.6 = (f32[64,256]{1,0:T(8,128)S(1)}, f32[64,256]{1,0:T(8,128)S(1)}, u32[]{:S(2)}, u32[]{:S(2)}) collective-permute-start(f32[64,256]{1,0:T(8,128)S(1)} %shard_map.114.refs_0_), channel_id=1, source_target_pairs={{0,1},{1,0},{2,3},{3,2},{4,5},{5,4},{6,7},{7,6},{8,9},{9,8},{10,11... | collective-permute-start | bytes 196616 | tf_op jit(solution)/shard_map/ppermute | solution.py:33
  17.7 9.0 %collective-permute-start.7 = (f32[64,256]{1,0:T(8,128)S(1)}, f32[64,256]{1,0:T(8,128)S(1)}, u32[]{:S(2)}, u32[]{:S(2)}) collective-permute-start(f32[64,256]{1,0:T(8,128)S(1)} %shard_map.114.refs_0_), channel_id=1, source_target_pairs={{0,2},{1,3},{2,0},{3,1},{4,6},{5,7},{6,4},{7,5},{8,10},{9,11},{10,... | collective-permute-start | bytes 196616 | tf_op jit(solution)/shard_map/ppermute | solution.py:33
  19.8 6.9 %collective-permute-start.8 = (f32[64,256]{1,0:T(8,128)S(1)}, f32[64,256]{1,0:T(8,128)S(1)}, u32[]{:S(2)}, u32[]{:S(2)}) collective-permute-start(f32[64,256]{1,0:T(8,128)S(1)} %shard_map.114.refs_0_), channel_id=1, source_target_pairs={{0,3},{1,2},{2,1},{3,0},{4,7},{5,6},{6,5},{7,4},{8,11},{9,10},{10,... | collective-permute-start | bytes 196616 | tf_op jit(solution)/shard_map/ppermute | solution.py:33
  21.7 12.5 %collective-permute-start.11 = (f32[64,256]{1,0:T(8,128)S(1)}, f32[64,256]{1,0:T(8,128)S(1)}, u32[]{:S(2)}, u32[]{:S(2)}) collective-permute-start(f32[64,256]{1,0:T(8,128)S(1)} %shard_map.115.refs_1_), channel_id=1, source_target_pairs={{0,3},{1,2},{2,1},{3,0},{4,7},{5,6},{6,5},{7,4},{8,11},{9,10},{10,... | collective-permute-start | bytes 196616 | tf_op jit(solution)/shard_map/ppermute | solution.py:33
  24.2 10.0 %collective-permute-start.12 = (f32[64,256]{1,0:T(8,128)S(1)}, f32[64,256]{1,0:T(8,128)S(1)}, u32[]{:S(2)}, u32[]{:S(2)}) collective-permute-start(f32[64,256]{1,0:T(8,128)S(1)} %shard_map.115.refs_1_), channel_id=1, source_target_pairs={{0,2},{1,3},{2,0},{3,1},{4,6},{5,7},{6,4},{7,5},{8,10},{9,11},{10,... | collective-permute-start | bytes 196616 | tf_op jit(solution)/shard_map/ppermute | solution.py:33
  24.3 9.7 %collective-permute-start.9 = (f32[64,256]{1,0:T(8,128)S(1)}, f32[64,256]{1,0:T(8,128)S(1)}, u32[]{:S(2)}, u32[]{:S(2)}) collective-permute-start(f32[64,256]{1,0:T(8,128)S(1)} %shard_map.115.refs_1_), channel_id=1, source_target_pairs={{0,1},{1,0},{2,3},{3,2},{4,5},{5,4},{6,7},{7,6},{8,9},{9,8},{10,11... | collective-permute-start | bytes 196616 | tf_op jit(solution)/shard_map/ppermute | solution.py:33
  27.4 13.3 %collective-permute-start.13 = (f32[64,256]{1,0:T(8,128)S(1)}, f32[64,256]{1,0:T(8,128)S(1)}, u32[]{:S(2)}, u32[]{:S(2)}) collective-permute-start(f32[64,256]{1,0:T(8,128)S(1)} %get-tuple-element.54), channel_id=1, source_target_pairs={{0,2},{1,3},{2,0},{3,1},{4,6},{5,7},{6,4},{7,5},{8,10},{9,11},{10,... | collective-permute-start | bytes 196616 | tf_op jit(solution)/shard_map/ppermute | solution.py:33
  33.5 7.2 %collective-permute-start.14 = (f32[64,256]{1,0:T(8,128)S(1)}, f32[64,256]{1,0:T(8,128)S(1)}, u32[]{:S(2)}, u32[]{:S(2)}) collective-permute-start(f32[64,256]{1,0:T(8,128)S(1)} %get-tuple-element.54), channel_id=1, source_target_pairs={{0,3},{1,2},{2,1},{3,0},{4,7},{5,6},{6,5},{7,4},{8,11},{9,10},{10,... | collective-permute-start | bytes 196616 | tf_op jit(solution)/shard_map/ppermute | solution.py:33
  34.0 5.1 %collective-permute-start.10 = (f32[64,256]{1,0:T(8,128)S(1)}, f32[64,256]{1,0:T(8,128)S(1)}, u32[]{:S(2)}, u32[]{:S(2)}) collective-permute-start(f32[64,256]{1,0:T(8,128)S(1)} %get-tuple-element.54), channel_id=1, source_target_pairs={{0,1},{1,0},{2,3},{3,2},{4,5},{5,4},{6,7},{7,6},{8,9},{9,8},{10,11... | collective-permute-start | bytes 196616 | tf_op jit(solution)/shard_map/ppermute | solution.py:33
  34.9 11.5 %collective-permute-start.16 = (f32[64,256]{1,0:T(8,128)S(1)}, f32[64,256]{1,0:T(8,128)S(1)}, u32[]{:S(2)}, u32[]{:S(2)}) collective-permute-start(f32[64,256]{1,0:T(8,128)S(1)} %get-tuple-element.56), channel_id=1, source_target_pairs={{0,3},{1,2},{2,1},{3,0},{4,7},{5,6},{6,5},{7,4},{8,11},{9,10},{10,... | collective-permute-start | bytes 196616 | tf_op jit(solution)/shard_map/ppermute | solution.py:33
  38.1 8.3 %collective-permute-start.17 = (f32[64,256]{1,0:T(8,128)S(1)}, f32[64,256]{1,0:T(8,128)S(1)}, u32[]{:S(2)}, u32[]{:S(2)}) collective-permute-start(f32[64,256]{1,0:T(8,128)S(1)} %get-tuple-element.56), channel_id=1, source_target_pairs={{0,2},{1,3},{2,0},{3,1},{4,6},{5,7},{6,4},{7,5},{8,10},{9,11},{10,... | collective-permute-start | bytes 196616 | tf_op jit(solution)/shard_map/ppermute | solution.py:33
  39.0 6.7 %collective-permute-start.15 = (f32[64,256]{1,0:T(8,128)S(1)}, f32[64,256]{1,0:T(8,128)S(1)}, u32[]{:S(2)}, u32[]{:S(2)}) collective-permute-start(f32[64,256]{1,0:T(8,128)S(1)} %get-tuple-element.56), channel_id=1, source_target_pairs={{0,1},{1,0},{2,3},{3,2},{4,5},{5,4},{6,7},{7,6},{8,9},{9,8},{10,11... | collective-permute-start | bytes 196616 | tf_op jit(solution)/shard_map/ppermute | solution.py:33
  41.4 11.5 %collective-permute-start.19 = (f32[64,256]{1,0:T(8,128)S(1)}, f32[64,256]{1,0:T(8,128)S(1)}, u32[]{:S(2)}, u32[]{:S(2)}) collective-permute-start(f32[64,256]{1,0:T(8,128)S(1)} %get-tuple-element.58.refs_2_), channel_id=1, source_target_pairs={{0,2},{1,3},{2,0},{3,1},{4,6},{5,7},{6,4},{7,5},{8,10},{9,11},{10,... | collective-permute-start | bytes 196616 | tf_op jit(solution)/shard_map/ppermute | solution.py:33
  45.7 7.2 %collective-permute-start.20 = (f32[64,256]{1,0:T(8,128)S(1)}, f32[64,256]{1,0:T(8,128)S(1)}, u32[]{:S(2)}, u32[]{:S(2)}) collective-permute-start(f32[64,256]{1,0:T(8,128)S(1)} %get-tuple-element.58.refs_2_), channel_id=1, source_target_pairs={{0,3},{1,2},{2,1},{3,0},{4,7},{5,6},{6,5},{7,4},{8,11},{9,10},{10,... | collective-permute-start | bytes 196616 | tf_op jit(solution)/shard_map/ppermute | solution.py:33
  45.7 5.3 %collective-permute-start.18 = (f32[64,256]{1,0:T(8,128)S(1)}, f32[64,256]{1,0:T(8,128)S(1)}, u32[]{:S(2)}, u32[]{:S(2)}) collective-permute-start(f32[64,256]{1,0:T(8,128)S(1)} %get-tuple-element.58.refs_2_), channel_id=1, source_target_pairs={{0,1},{1,0},{2,3},{3,2},{4,5},{5,4},{6,7},{7,6},{8,9},{9,8},{10,11... | collective-permute-start | bytes 196616 | tf_op jit(solution)/shard_map/ppermute | solution.py:33
  47.1 12.0 %collective-permute-start.23 = (f32[64,256]{1,0:T(8,128)S(1)}, f32[64,256]{1,0:T(8,128)S(1)}, u32[]{:S(2)}, u32[]{:S(2)}) collective-permute-start(f32[64,256]{1,0:T(8,128)S(1)} %get-tuple-element.60.refs_3_), channel_id=1, source_target_pairs={{0,3},{1,2},{2,1},{3,0},{4,7},{5,6},{6,5},{7,4},{8,11},{9,10},{10,... | collective-permute-start | bytes 196616 | tf_op jit(solution)/shard_map/ppermute | solution.py:33
  50.8 8.3 %collective-permute-start.24 = (f32[64,256]{1,0:T(8,128)S(1)}, f32[64,256]{1,0:T(8,128)S(1)}, u32[]{:S(2)}, u32[]{:S(2)}) collective-permute-start(f32[64,256]{1,0:T(8,128)S(1)} %get-tuple-element.60.refs_3_), channel_id=1, source_target_pairs={{0,2},{1,3},{2,0},{3,1},{4,6},{5,7},{6,4},{7,5},{8,10},{9,11},{10,... | collective-permute-start | bytes 196616 | tf_op jit(solution)/shard_map/ppermute | solution.py:33
  51.0 7.4 %collective-permute-start.21 = (f32[64,256]{1,0:T(8,128)S(1)}, f32[64,256]{1,0:T(8,128)S(1)}, u32[]{:S(2)}, u32[]{:S(2)}) collective-permute-start(f32[64,256]{1,0:T(8,128)S(1)} %get-tuple-element.60.refs_3_), channel_id=1, source_target_pairs={{0,1},{1,0},{2,3},{3,2},{4,5},{5,4},{6,7},{7,6},{8,9},{9,8},{10,11... | collective-permute-start | bytes 196616 | tf_op jit(solution)/shard_map/ppermute | solution.py:33
  53.6 11.4 %collective-permute-start.25 = (f32[64,256]{1,0:T(8,128)S(1)}, f32[64,256]{1,0:T(8,128)S(1)}, u32[]{:S(2)}, u32[]{:S(2)}) collective-permute-start(f32[64,256]{1,0:T(8,128)S(1)} %get-tuple-element.62), channel_id=1, source_target_pairs={{0,2},{1,3},{2,0},{3,1},{4,6},{5,7},{6,4},{7,5},{8,10},{9,11},{10,... | collective-permute-start | bytes 196616 | tf_op jit(solution)/shard_map/ppermute | solution.py:33
  58.4 6.6 %collective-permute-start.26 = (f32[64,256]{1,0:T(8,128)S(1)}, f32[64,256]{1,0:T(8,128)S(1)}, u32[]{:S(2)}, u32[]{:S(2)}) collective-permute-start(f32[64,256]{1,0:T(8,128)S(1)} %get-tuple-element.62), channel_id=1, source_target_pairs={{0,3},{1,2},{2,1},{3,0},{4,7},{5,6},{6,5},{7,4},{8,11},{9,10},{10,... | collective-permute-start | bytes 196616 | tf_op jit(solution)/shard_map/ppermute | solution.py:33
  58.4 6.1 %collective-permute-start.22 = (f32[64,256]{1,0:T(8,128)S(1)}, f32[64,256]{1,0:T(8,128)S(1)}, u32[]{:S(2)}, u32[]{:S(2)}) collective-permute-start(f32[64,256]{1,0:T(8,128)S(1)} %get-tuple-element.62), channel_id=1, source_target_pairs={{0,1},{1,0},{2,3},{3,2},{4,5},{5,4},{6,7},{7,6},{8,9},{9,8},{10,11... | collective-permute-start | bytes 196616 | tf_op jit(solution)/shard_map/ppermute | solution.py:33
  59.8 10.7 %collective-permute-start.28 = (f32[64,256]{1,0:T(8,128)S(1)}, f32[64,256]{1,0:T(8,128)S(1)}, u32[]{:S(2)}, u32[]{:S(2)}) collective-permute-start(f32[64,256]{1,0:T(8,128)S(1)} %get-tuple-element.64), channel_id=1, source_target_pairs={{0,3},{1,2},{2,1},{3,0},{4,7},{5,6},{6,5},{7,4},{8,11},{9,10},{10,... | collective-permute-start | bytes 196616 | tf_op jit(solution)/shard_map/ppermute | solution.py:33
  63.9 9.5 %collective-permute-start.29 = (f32[64,256]{1,0:T(8,128)S(1)}, f32[64,256]{1,0:T(8,128)S(1)}, u32[]{:S(2)}, u32[]{:S(2)}) collective-permute-start(f32[64,256]{1,0:T(8,128)S(1)} %get-tuple-element.64), channel_id=1, source_target_pairs={{0,2},{1,3},{2,0},{3,1},{4,6},{5,7},{6,4},{7,5},{8,10},{9,11},{10,... | collective-permute-start | bytes 196616 | tf_op jit(solution)/shard_map/ppermute | solution.py:33
  64.5 5.3 %collective-permute-start.27 = (f32[64,256]{1,0:T(8,128)S(1)}, f32[64,256]{1,0:T(8,128)S(1)}, u32[]{:S(2)}, u32[]{:S(2)}) collective-permute-start(f32[64,256]{1,0:T(8,128)S(1)} %get-tuple-element.64), channel_id=1, source_target_pairs={{0,1},{1,0},{2,3},{3,2},{4,5},{5,4},{6,7},{7,6},{8,9},{9,8},{10,11... | collective-permute-start | bytes 196616 | tf_op jit(solution)/shard_map/ppermute | solution.py:33
  65.7 12.8 %collective-permute-start.31 = (f32[64,256]{1,0:T(8,128)S(1)}, f32[64,256]{1,0:T(8,128)S(1)}, u32[]{:S(2)}, u32[]{:S(2)}) collective-permute-start(f32[64,256]{1,0:T(8,128)S(1)} %get-tuple-element.66.refs_4_), channel_id=1, source_target_pairs={{0,2},{1,3},{2,0},{3,1},{4,6},{5,7},{6,4},{7,5},{8,10},{9,11},{10,... | collective-permute-start | bytes 196616 | tf_op jit(solution)/shard_map/ppermute | solution.py:33
  69.8 8.8 %collective-permute-start.32 = (f32[64,256]{1,0:T(8,128)S(1)}, f32[64,256]{1,0:T(8,128)S(1)}, u32[]{:S(2)}, u32[]{:S(2)}) collective-permute-start(f32[64,256]{1,0:T(8,128)S(1)} %get-tuple-element.66.refs_4_), channel_id=1, source_target_pairs={{0,3},{1,2},{2,1},{3,0},{4,7},{5,6},{6,5},{7,4},{8,11},{9,10},{10,... | collective-permute-start | bytes 196616 | tf_op jit(solution)/shard_map/ppermute | solution.py:33
  69.8 6.1 %collective-permute-start.30 = (f32[64,256]{1,0:T(8,128)S(1)}, f32[64,256]{1,0:T(8,128)S(1)}, u32[]{:S(2)}, u32[]{:S(2)}) collective-permute-start(f32[64,256]{1,0:T(8,128)S(1)} %get-tuple-element.66.refs_4_), channel_id=1, source_target_pairs={{0,1},{1,0},{2,3},{3,2},{4,5},{5,4},{6,7},{7,6},{8,9},{9,8},{10,11... | collective-permute-start | bytes 196616 | tf_op jit(solution)/shard_map/ppermute | solution.py:33
  74.1 9.4 %collective-permute-start.35 = (f32[64,256]{1,0:T(8,128)S(1)}, f32[64,256]{1,0:T(8,128)S(1)}, u32[]{:S(2)}, u32[]{:S(2)}) collective-permute-start(f32[64,256]{1,0:T(8,128)S(1)} %get-tuple-element.68.refs_5_), channel_id=1, source_target_pairs={{0,3},{1,2},{2,1},{3,0},{4,7},{5,6},{6,5},{7,4},{8,11},{9,10},{10,... | collective-permute-start | bytes 196616 | tf_op jit(solution)/shard_map/ppermute | solution.py:33
  75.9 8.4 %collective-permute-start.36 = (f32[64,256]{1,0:T(8,128)S(1)}, f32[64,256]{1,0:T(8,128)S(1)}, u32[]{:S(2)}, u32[]{:S(2)}) collective-permute-start(f32[64,256]{1,0:T(8,128)S(1)} %get-tuple-element.68.refs_5_), channel_id=1, source_target_pairs={{0,2},{1,3},{2,0},{3,1},{4,6},{5,7},{6,4},{7,5},{8,10},{9,11},{10,... | collective-permute-start | bytes 196616 | tf_op jit(solution)/shard_map/ppermute | solution.py:33
  75.9 6.0 %collective-permute-start.33 = (f32[64,256]{1,0:T(8,128)S(1)}, f32[64,256]{1,0:T(8,128)S(1)}, u32[]{:S(2)}, u32[]{:S(2)}) collective-permute-start(f32[64,256]{1,0:T(8,128)S(1)} %get-tuple-element.68.refs_5_), channel_id=1, source_target_pairs={{0,1},{1,0},{2,3},{3,2},{4,5},{5,4},{6,7},{7,6},{8,9},{9,8},{10,11... | collective-permute-start | bytes 196616 | tf_op jit(solution)/shard_map/ppermute | solution.py:33
  79.3 10.3 %collective-permute-start.37 = (f32[64,256]{1,0:T(8,128)S(1)}, f32[64,256]{1,0:T(8,128)S(1)}, u32[]{:S(2)}, u32[]{:S(2)}) collective-permute-start(f32[64,256]{1,0:T(8,128)S(1)} %get-tuple-element.70), channel_id=1, source_target_pairs={{0,2},{1,3},{2,0},{3,1},{4,6},{5,7},{6,4},{7,5},{8,10},{9,11},{10,... | collective-permute-start | bytes 196616 | tf_op jit(solution)/shard_map/ppermute | solution.py:33
  79.8 9.7 %collective-permute-start.38 = (f32[64,256]{1,0:T(8,128)S(1)}, f32[64,256]{1,0:T(8,128)S(1)}, u32[]{:S(2)}, u32[]{:S(2)}) collective-permute-start(f32[64,256]{1,0:T(8,128)S(1)} %get-tuple-element.70), channel_id=1, source_target_pairs={{0,3},{1,2},{2,1},{3,0},{4,7},{5,6},{6,5},{7,4},{8,11},{9,10},{10,... | collective-permute-start | bytes 196616 | tf_op jit(solution)/shard_map/ppermute | solution.py:33
  81.9 6.1 %collective-permute-start.34 = (f32[64,256]{1,0:T(8,128)S(1)}, f32[64,256]{1,0:T(8,128)S(1)}, u32[]{:S(2)}, u32[]{:S(2)}) collective-permute-start(f32[64,256]{1,0:T(8,128)S(1)} %get-tuple-element.70), channel_id=1, source_target_pairs={{0,1},{1,0},{2,3},{3,2},{4,5},{5,4},{6,7},{7,6},{8,9},{9,8},{10,11... | collective-permute-start | bytes 196616 | tf_op jit(solution)/shard_map/ppermute | solution.py:33
  85.1 9.1 %collective-permute-start.40 = (f32[64,256]{1,0:T(8,128)S(1)}, f32[64,256]{1,0:T(8,128)S(1)}, u32[]{:S(2)}, u32[]{:S(2)}) collective-permute-start(f32[64,256]{1,0:T(8,128)S(1)} %get-tuple-element.72), channel_id=1, source_target_pairs={{0,3},{1,2},{2,1},{3,0},{4,7},{5,6},{6,5},{7,4},{8,11},{9,10},{10,... | collective-permute-start | bytes 196616 | tf_op jit(solution)/shard_map/ppermute | solution.py:33
  88.0 6.2 %collective-permute-start.41 = (f32[64,256]{1,0:T(8,128)S(1)}, f32[64,256]{1,0:T(8,128)S(1)}, u32[]{:S(2)}, u32[]{:S(2)}) collective-permute-start(f32[64,256]{1,0:T(8,128)S(1)} %get-tuple-element.72), channel_id=1, source_target_pairs={{0,2},{1,3},{2,0},{3,1},{4,6},{5,7},{6,4},{7,5},{8,10},{9,11},{10,... | collective-permute-start | bytes 196616 | tf_op jit(solution)/shard_map/ppermute | solution.py:33
  88.0 5.6 %collective-permute-start.39 = (f32[64,256]{1,0:T(8,128)S(1)}, f32[64,256]{1,0:T(8,128)S(1)}, u32[]{:S(2)}, u32[]{:S(2)}) collective-permute-start(f32[64,256]{1,0:T(8,128)S(1)} %get-tuple-element.72), channel_id=1, source_target_pairs={{0,1},{1,0},{2,3},{3,2},{4,5},{5,4},{6,7},{7,6},{8,9},{9,8},{10,11... | collective-permute-start | bytes 196616 | tf_op jit(solution)/shard_map/ppermute | solution.py:33
  90.3 9.1 %collective-permute-start.43 = (f32[64,256]{1,0:T(8,128)S(1)}, f32[64,256]{1,0:T(8,128)S(1)}, u32[]{:S(2)}, u32[]{:S(2)}) collective-permute-start(f32[64,256]{1,0:T(8,128)S(1)} %get-tuple-element.74.refs_6_), channel_id=1, source_target_pairs={{0,2},{1,3},{2,0},{3,1},{4,6},{5,7},{6,4},{7,5},{8,10},{9,11},{10,... | collective-permute-start | bytes 196616 | tf_op jit(solution)/shard_map/ppermute | solution.py:33
  91.7 7.7 %collective-permute-start.44 = (f32[64,256]{1,0:T(8,128)S(1)}, f32[64,256]{1,0:T(8,128)S(1)}, u32[]{:S(2)}, u32[]{:S(2)}) collective-permute-start(f32[64,256]{1,0:T(8,128)S(1)} %get-tuple-element.74.refs_6_), channel_id=1, source_target_pairs={{0,3},{1,2},{2,1},{3,0},{4,7},{5,6},{6,5},{7,4},{8,11},{9,10},{10,... | collective-permute-start | bytes 196616 | tf_op jit(solution)/shard_map/ppermute | solution.py:33
  93.6 5.0 %collective-permute-start.42 = (f32[64,256]{1,0:T(8,128)S(1)}, f32[64,256]{1,0:T(8,128)S(1)}, u32[]{:S(2)}, u32[]{:S(2)}) collective-permute-start(f32[64,256]{1,0:T(8,128)S(1)} %get-tuple-element.74.refs_6_), channel_id=1, source_target_pairs={{0,1},{1,0},{2,3},{3,2},{4,5},{5,4},{6,7},{7,6},{8,9},{9,8},{10,11... | collective-permute-start | bytes 196616 | tf_op jit(solution)/shard_map/ppermute | solution.py:33
  94.9 8.6 %collective-permute-start.46 = (f32[64,256]{1,0:T(8,128)S(1)}, f32[64,256]{1,0:T(8,128)S(1)}, u32[]{:S(2)}, u32[]{:S(2)}) collective-permute-start(f32[64,256]{1,0:T(8,128)S(1)} %get-tuple-element.76.refs_7_), channel_id=1, source_target_pairs={{0,3},{1,2},{2,1},{3,0},{4,7},{5,6},{6,5},{7,4},{8,11},{9,10},{10,... | collective-permute-start | bytes 196616 | tf_op jit(solution)/shard_map/ppermute | solution.py:33
  97.5 6.1 %collective-permute-start.47 = (f32[64,256]{1,0:T(8,128)S(1)}, f32[64,256]{1,0:T(8,128)S(1)}, u32[]{:S(2)}, u32[]{:S(2)}) collective-permute-start(f32[64,256]{1,0:T(8,128)S(1)} %get-tuple-element.76.refs_7_), channel_id=1, source_target_pairs={{0,2},{1,3},{2,0},{3,1},{4,6},{5,7},{6,4},{7,5},{8,10},{9,11},{10,... | collective-permute-start | bytes 196616 | tf_op jit(solution)/shard_map/ppermute | solution.py:33
  98.6 4.9 %collective-permute-start.45 = (f32[64,256]{1,0:T(8,128)S(1)}, f32[64,256]{1,0:T(8,128)S(1)}, u32[]{:S(2)}, u32[]{:S(2)}) collective-permute-start(f32[64,256]{1,0:T(8,128)S(1)} %get-tuple-element.76.refs_7_), channel_id=1, source_target_pairs={{0,1},{1,0},{2,3},{3,2},{4,5},{5,4},{6,7},{7,6},{8,9},{9,8},{10,11... | collective-permute-start | bytes 196616 | tf_op jit(solution)/shard_map/ppermute | solution.py:33
  99.5 18.0 %copy-start.1 = (f32[2,256,1024]{2,1,0:T(8,128)S(1)}, f32[2,256,1024]{2,1,0:T(8,128)}, u32[]{:S(2)}) copy-start(f32[2,256,1024]{2,1,0:T(8,128)} %refs_0_.1) | copy-start | bytes 6291460
  99.5 18.0 %copy-start.4 = (f32[1,256,1024]{2,1,0:T(8,128)S(1)}, f32[1,256,1024]{2,1,0:T(8,128)}, u32[]{:S(2)}) copy-start(f32[1,256,1024]{2,1,0:T(8,128)} %refs_1_.1) | copy-start | bytes 3145732
  104.8 1.4 %collective-permute-start.48 = (f32[4,16,512]{2,1,0:T(8,128)S(1)}, f32[4,16,512]{2,1,0:T(8,128)S(1)}, u32[]{:S(2)}, u32[]{:S(2)}) collective-permute-start(f32[4,16,512]{2,1,0:T(8,128)S(1)} %get-tuple-element.80), channel_id=1, source_target_pairs={{0,4},{4,0},{8,12},{12,8},{16,20},{20,16},{24,28},{28,24},{1,5},{5... | collective-permute-start | bytes 393224 | tf_op jit(solution)/shard_map/ppermute | solution.py:289
  106.2 5.3 %collective-permute-start.49 = (f32[2,16,512]{2,1,0:T(8,128)S(1)}, f32[2,16,512]{2,1,0:T(8,128)S(1)}, u32[]{:S(2)}, u32[]{:S(2)}) collective-permute-start(f32[2,16,512]{2,1,0:T(8,128)S(1)} %get-tuple-element.82), channel_id=1, source_target_pairs={{0,24},{4,28},{8,16},{12,20},{16,8},{20,12},{24,0},{28,4},{1,25},{... | collective-permute-start | bytes 196616 | tf_op jit(solution)/shard_map/ppermute | solution.py:89
  108.4 4.4 %collective-permute-start.50 = (f32[2,16,512]{2,1,0:T(8,128)S(1)}, f32[2,16,512]{2,1,0:T(8,128)S(1)}, u32[]{:S(2)}, u32[]{:S(2)}) collective-permute-start(f32[2,16,512]{2,1,0:T(8,128)S(1)} %get-tuple-element.83), channel_id=1, source_target_pairs={{0,16},{4,20},{8,24},{12,28},{16,0},{20,4},{24,8},{28,12},{1,17},{... | collective-permute-start | bytes 196616 | tf_op jit(solution)/shard_map/ppermute | solution.py:89
  109.2 4.3 %collective-permute-start.51 = (f32[2,16,512]{2,1,0:T(8,128)S(1)}, f32[2,16,512]{2,1,0:T(8,128)S(1)}, u32[]{:S(2)}, u32[]{:S(2)}) collective-permute-start(f32[2,16,512]{2,1,0:T(8,128)S(1)} %get-tuple-element.84), channel_id=1, source_target_pairs={{0,8},{4,12},{8,0},{12,4},{16,24},{20,28},{24,16},{28,20},{1,9},{5... | collective-permute-start | bytes 196616 | tf_op jit(solution)/shard_map/ppermute | solution.py:89
  113.9 7.9 %collective-permute-start.52 = (f32[16,1280]{1,0:T(8,128)S(1)}, f32[16,1280]{1,0:T(8,128)S(1)}, u32[]{:S(2)}, u32[]{:S(2)}) collective-permute-start(f32[16,1280]{1,0:T(8,128)S(1)} %get-tuple-element.87), channel_id=1, source_target_pairs={{0,2},{1,3},{2,0},{3,1},{4,6},{5,7},{6,4},{7,5},{8,10},{9,11},{10,... | collective-permute-start | bytes 245768 | tf_op jit(solution)/shard_map/ppermute | solution.py:33
  115.2 6.6 %collective-permute-start.53 = (f32[16,1280]{1,0:T(8,128)S(1)}, f32[16,1280]{1,0:T(8,128)S(1)}, u32[]{:S(2)}, u32[]{:S(2)}) collective-permute-start(f32[16,1280]{1,0:T(8,128)S(1)} %get-tuple-element.88), channel_id=1, source_target_pairs={{0,3},{1,2},{2,1},{3,0},{4,7},{5,6},{6,5},{7,4},{8,11},{9,10},{10,... | collective-permute-start | bytes 245768 | tf_op jit(solution)/shard_map/ppermute | solution.py:33
  116.5 6.0 %collective-permute-start.54 = (f32[16,1280]{1,0:T(8,128)S(1)}, f32[16,1280]{1,0:T(8,128)S(1)}, u32[]{:S(2)}, u32[]{:S(2)}) collective-permute-start(f32[16,1280]{1,0:T(8,128)S(1)} %get-tuple-element.89), channel_id=1, source_target_pairs={{0,1},{1,0},{2,3},{3,2},{4,5},{5,4},{6,7},{7,6},{8,9},{9,8},{10,11... | collective-permute-start | bytes 245768 | tf_op jit(solution)/shard_map/ppermute | solution.py:33
  122.9 4.7 %collective-permute-start.55 = (f32[16,256]{1,0:T(8,128)S(1)}, f32[16,256]{1,0:T(8,128)S(1)}, u32[]{:S(2)}, u32[]{:S(2)}) collective-permute-start(f32[16,256]{1,0:T(8,128)S(1)} %get-tuple-element.92.refs_0_.refs_6_), channel_id=1, source_target_pairs={{0,2},{1,3},{2,0},{3,1},{4,6},{5,7},{6,4},{7,5},{8,10},{9,11},{10,... | collective-permute-start | bytes 49160 | tf_op jit(solution)/shard_map/ppermute | solution.py:33
  124.1 5.5 %collective-permute-start.56 = (f32[16,256]{1,0:T(8,128)S(1)}, f32[16,256]{1,0:T(8,128)S(1)}, u32[]{:S(2)}, u32[]{:S(2)}) collective-permute-start(f32[16,256]{1,0:T(8,128)S(1)} %get-tuple-element.92.refs_0_.refs_6_), channel_id=1, source_target_pairs={{0,3},{1,2},{2,1},{3,0},{4,7},{5,6},{6,5},{7,4},{8,11},{9,10},{10,... | collective-permute-start | bytes 49160 | tf_op jit(solution)/shard_map/ppermute | solution.py:33
  125.9 3.9 %collective-permute-start.57 = (f32[16,256]{1,0:T(8,128)S(1)}, f32[16,256]{1,0:T(8,128)S(1)}, u32[]{:S(2)}, u32[]{:S(2)}) collective-permute-start(f32[16,256]{1,0:T(8,128)S(1)} %get-tuple-element.92.refs_0_.refs_6_), channel_id=1, source_target_pairs={{0,1},{1,0},{2,3},{3,2},{4,5},{5,4},{6,7},{7,6},{8,9},{9,8},{10,11... | collective-permute-start | bytes 49160 | tf_op jit(solution)/shard_map/ppermute | solution.py:33
  130.2 4.7 %collective-permute-start.58 = (f32[16,256]{1,0:T(8,128)S(1)}, f32[16,256]{1,0:T(8,128)S(1)}, u32[]{:S(2)}, u32[]{:S(2)}) collective-permute-start(f32[16,256]{1,0:T(8,128)S(1)} %shard_map.124.refs_0_), channel_id=1, source_target_pairs={{0,2},{1,3},{2,0},{3,1},{4,6},{5,7},{6,4},{7,5},{8,10},{9,11},{10,... | collective-permute-start | bytes 49160 | tf_op jit(solution)/shard_map/ppermute | solution.py:33
  130.8 5.5 %collective-permute-start.59 = (f32[16,256]{1,0:T(8,128)S(1)}, f32[16,256]{1,0:T(8,128)S(1)}, u32[]{:S(2)}, u32[]{:S(2)}) collective-permute-start(f32[16,256]{1,0:T(8,128)S(1)} %shard_map.124.refs_0_), channel_id=1, source_target_pairs={{0,3},{1,2},{2,1},{3,0},{4,7},{5,6},{6,5},{7,4},{8,11},{9,10},{10,... | collective-permute-start | bytes 49160 | tf_op jit(solution)/shard_map/ppermute | solution.py:33
  132.9 3.7 %collective-permute-start.60 = (f32[16,256]{1,0:T(8,128)S(1)}, f32[16,256]{1,0:T(8,128)S(1)}, u32[]{:S(2)}, u32[]{:S(2)}) collective-permute-start(f32[16,256]{1,0:T(8,128)S(1)} %shard_map.124.refs_0_), channel_id=1, source_target_pairs={{0,1},{1,0},{2,3},{3,2},{4,5},{5,4},{6,7},{7,6},{8,9},{9,8},{10,11... | collective-permute-start | bytes 49160 | tf_op jit(solution)/shard_map/ppermute | solution.py:33
  (7 other events, 87.7 us)

commit v19 on v18

--- a/solution.py
+++ b/solution.py
@@ -33,7 +33,7 @@
     return lax.ppermute(value, axis, pairs)
 
 
-def gather_rows(value, ties=(), swapped=False, far_first=False):
+def gather_rows(value, ties=(), far_first=False):
     members = lax.axis_size("grp")
     me = lax.axis_index("grp")
     rows = value.shape[1]
@@ -41,8 +41,6 @@
     distances = list(range(1, members))
     if far_first:
         distances = distances[1:] + distances[:1]
-    if swapped:
-        distances[1:3] = distances[2:0:-1]
     for distance in distances:
         owner = partner(me, distance, members)
         tied = value
@@ -54,12 +52,6 @@
 
 def gather_far_first(value):
     return [piece for _, piece in gather_rows(value, far_first=True)]
-
-
-def gather_sorted(pieces, swapped):
-    if swapped:
-        return pieces[:2] + pieces[3:1:-1] + pieces[4:]
-    return pieces
 
 
 def assemble(pieces, order):
@@ -469,7 +461,7 @@
         for i in range(streams):
             turn_taken = step > 0 and last is not None
             ties = [(1, last[0][1][1])] if step * streams + i > streams else []
-            pieces = gather_rows(values[i], ties, i % 2 == 1)
+            pieces = gather_rows(values[i], ties)
             if step == 1 and i == 0:
                 later = turn(rhs_local, 1, supernodes, streams, pieces[1][1])
             if turn_taken:
@@ -477,7 +469,7 @@
                 pieces[1] = (offset, lax.optimization_barrier((piece, last[1]))[0])
             if step == 0:
                 owned = apply_split(
-                    [p for _, p in gather_sorted(pieces, i % 2 == 1)],
+                    [p for _, p in pieces],
                     first_top,
                     first_rest,
                     0,

time: 138 us -> 137 us (level)
  starting transfers between devices: 94.2 us -> 90.7 us
  waiting for transfers between devices: 23 us -> 25.2 us
    ppermute x57, starting transfers between devices: 90.6 us -> 87.1 us  [send(): return lax.ppermute(value, axis, pairs)]
    ppermute x57, waiting for transfers between devices: 19 us -> 21.2 us  [send(): return lax.ppermute(value, axis, pairs)]
  transfers between devices with their start and end apart: 61 -> 61, of which waited for: 19 -> 21; matrix products, arithmetic and copies ran while one was open for 7% -> 7% of each run, Pallas kernels for 3% -> 3%
where the time goes in v19:
time: 137 us; the launch traced here: 136 us
  starting transfers between devices  90.7 us (66%)
  waiting for transfers between devices  25.2 us (18%)
  matrix products  7.54 us (6%)
  Pallas kernels  7.51 us (5%)
  between operations  2.13 us (2%)
  local copies, waits for them, and re-layouts  1.82 us (1%)
  other arithmetic  1.41 us (1%)
    ppermute x57, starting transfers between devices, send(): return lax.ppermute(value, axis, pairs)  87.1 us
    ppermute x57, waiting for transfers between devices, send(): return lax.ppermute(value, axis, pairs)  21.2 us
    dot_general x12, matrix products, contract_last(): lax.dot_general(left, right, (((left.ndim - 1,), (right.ndim - 1,)), ((),...  7.54 us
    pallas_call x13, Pallas kernels, local_kernel(): pl.pallas_call(body, out_shape=list(outs), in_specs=specs or [VMEM] * len...  7.51 us
    ppermute x3, starting transfers between devices, swap(): return lax.ppermute(value, axis, pairs)  3.55 us
    ppermute x3, waiting for transfers between devices, swap(): return lax.ppermute(value, axis, pairs)  2.74 us
  transfers between devices with their start and end apart: 61, of which 21 were waited for; matrix products, arithmetic and copies ran while one was open for 7% of the time, Pallas kernels for 3%

profile of v19, /device:TPU:0, one launch (start us, length us, event | category | flops | bytes accessed | tf_op | source)
XLA Modules:
  0.0 136.3 jit_solution(15951093821866406919)
XLA Ops:
  0.6 1.0 copy-done.2
  1.9 3.1 %collective-permute-start = (f32[64,256]{1,0:T(8,128)S(1)}, f32[64,256]{1,0:T(8,128)S(1)}, u32[]{:S(2)}, u32[]{:S(2)}) collective-permute-start(f32[64,256]{1,0:T(8,128)S(1)} %get-tuple-element.49.refs_0_), channel_id=1, source_target_pairs={{0,1},{1,0},{2,3},{3,2},{4,5},{5,4},{6,7},{7,6},{8,9},{9,8},{10,11... | collective-permute-start | bytes 196616 | tf_op jit(solution)/shard_map/ppermute | solution.py:33
  5.0 2.6 %collective-permute-start.1 = (f32[64,256]{1,0:T(8,128)S(1)}, f32[64,256]{1,0:T(8,128)S(1)}, u32[]{:S(2)}, u32[]{:S(2)}) collective-permute-start(f32[64,256]{1,0:T(8,128)S(1)} %get-tuple-element.49.refs_0_), channel_id=1, source_target_pairs={{0,2},{1,3},{2,0},{3,1},{4,6},{5,7},{6,4},{7,5},{8,10},{9,11},{10,... | collective-permute-start | bytes 196616 | tf_op jit(solution)/shard_map/ppermute | solution.py:33
  7.6 0.9 collective-permute-start.3
  8.5 3.5 %collective-permute-start.4 = (f32[64,256]{1,0:T(8,128)S(1)}, f32[64,256]{1,0:T(8,128)S(1)}, u32[]{:S(2)}, u32[]{:S(2)}) collective-permute-start(f32[64,256]{1,0:T(8,128)S(1)} %get-tuple-element.50.refs_0_), channel_id=1, source_target_pairs={{0,2},{1,3},{2,0},{3,1},{4,6},{5,7},{6,4},{7,5},{8,10},{9,11},{10,... | collective-permute-start | bytes 196616 | tf_op jit(solution)/shard_map/ppermute | solution.py:33
  12.0 1.4 %fusion = (bf16[1,256,1024]{2,1,0:T(8,128)(2,1)S(1)}, bf16[1,256,1024]{2,1,0:T(8,128)(2,1)S(1)}) fusion(f32[1,4,256,1024]{3,2,1,0:T(8,128)} %param.11), kind=kLoop, calls=%fused_computation.2 | loop fusion | flops 1048576 | bytes 2097152 | tf_op jit(solution)/shard_map/convert_element_type | solution.py:454
  14.6 3.0 %collective-permute-start.6 = (f32[64,256]{1,0:T(8,128)S(1)}, f32[64,256]{1,0:T(8,128)S(1)}, u32[]{:S(2)}, u32[]{:S(2)}) collective-permute-start(f32[64,256]{1,0:T(8,128)S(1)} %shard_map.114.refs_0_), channel_id=1, source_target_pairs={{0,1},{1,0},{2,3},{3,2},{4,5},{5,4},{6,7},{7,6},{8,9},{9,8},{10,11... | collective-permute-start | bytes 196616 | tf_op jit(solution)/shard_map/ppermute | solution.py:33
  17.7 2.1 %collective-permute-start.7 = (f32[64,256]{1,0:T(8,128)S(1)}, f32[64,256]{1,0:T(8,128)S(1)}, u32[]{:S(2)}, u32[]{:S(2)}) collective-permute-start(f32[64,256]{1,0:T(8,128)S(1)} %shard_map.114.refs_0_), channel_id=1, source_target_pairs={{0,2},{1,3},{2,0},{3,1},{4,6},{5,7},{6,4},{7,5},{8,10},{9,11},{10,... | collective-permute-start | bytes 196616 | tf_op jit(solution)/shard_map/ppermute | solution.py:33
  19.8 1.4 %collective-permute-start.8 = (f32[64,256]{1,0:T(8,128)S(1)}, f32[64,256]{1,0:T(8,128)S(1)}, u32[]{:S(2)}, u32[]{:S(2)}) collective-permute-start(f32[64,256]{1,0:T(8,128)S(1)} %shard_map.114.refs_0_), channel_id=1, source_target_pairs={{0,3},{1,2},{2,1},{3,0},{4,7},{5,6},{6,5},{7,4},{8,11},{9,10},{10,... | collective-permute-start | bytes 196616 | tf_op jit(solution)/shard_map/ppermute | solution.py:33
  21.7 2.3 %collective-permute-start.11 = (f32[64,256]{1,0:T(8,128)S(1)}, f32[64,256]{1,0:T(8,128)S(1)}, u32[]{:S(2)}, u32[]{:S(2)}) collective-permute-start(f32[64,256]{1,0:T(8,128)S(1)} %shard_map.115.refs_1_), channel_id=1, source_target_pairs={{0,2},{1,3},{2,0},{3,1},{4,6},{5,7},{6,4},{7,5},{8,10},{9,11},{10,... | collective-permute-start | bytes 196616 | tf_op jit(solution)/shard_map/ppermute | solution.py:33
  24.0 0.7 collective-permute-start.12
  25.8 2.1 %collective-permute-done.7 = f32[64,256]{1,0:T(8,128)S(1)} collective-permute-done((f32[64,256]{1,0:T(8,128)S(1)}, f32[64,256]{1,0:T(8,128)S(1)}, u32[]{:S(2)}, u32[]{:S(2)}) %collective-permute-start.7) | collective-permute-done | bytes 65568 | tf_op jit(solution)/shard_map/ppermute | solution.py:33
  28.0 0.6 constant_dynamic-update-slice_fusion.51
  28.6 4.3 %collective-permute-start.13 = (f32[64,256]{1,0:T(8,128)S(1)}, f32[64,256]{1,0:T(8,128)S(1)}, u32[]{:S(2)}, u32[]{:S(2)}) collective-permute-start(f32[64,256]{1,0:T(8,128)S(1)} %get-tuple-element.54), channel_id=1, source_target_pairs={{0,2},{1,3},{2,0},{3,1},{4,6},{5,7},{6,4},{7,5},{8,10},{9,11},{10,... | collective-permute-start | bytes 196616 | tf_op jit(solution)/shard_map/ppermute | solution.py:33
  33.6 0.6 constant_dynamic-update-slice_fusion.43
  34.2 3.8 %collective-permute-start.16 = (f32[64,256]{1,0:T(8,128)S(1)}, f32[64,256]{1,0:T(8,128)S(1)}, u32[]{:S(2)}, u32[]{:S(2)}) collective-permute-start(f32[64,256]{1,0:T(8,128)S(1)} %get-tuple-element.56), channel_id=1, source_target_pairs={{0,2},{1,3},{2,0},{3,1},{4,6},{5,7},{6,4},{7,5},{8,10},{9,11},{10,... | collective-permute-start | bytes 196616 | tf_op jit(solution)/shard_map/ppermute | solution.py:33
  38.7 1.1 collective-permute-start.15
  39.9 0.6 constant_dynamic-update-slice_fusion.39
  40.5 2.7 %collective-permute-start.19 = (f32[64,256]{1,0:T(8,128)S(1)}, f32[64,256]{1,0:T(8,128)S(1)}, u32[]{:S(2)}, u32[]{:S(2)}) collective-permute-start(f32[64,256]{1,0:T(8,128)S(1)} %get-tuple-element.58.refs_2_), channel_id=1, source_target_pairs={{0,2},{1,3},{2,0},{3,1},{4,6},{5,7},{6,4},{7,5},{8,10},{9,11},{10,... | collective-permute-start | bytes 196616 | tf_op jit(solution)/shard_map/ppermute | solution.py:33
  43.2 0.7 collective-permute-start.20
  43.9 0.6 collective-permute-start.18
  45.3 4.8 %collective-permute-start.23 = (f32[64,256]{1,0:T(8,128)S(1)}, f32[64,256]{1,0:T(8,128)S(1)}, u32[]{:S(2)}, u32[]{:S(2)}) collective-permute-start(f32[64,256]{1,0:T(8,128)S(1)} %get-tuple-element.60.refs_3_), channel_id=1, source_target_pairs={{0,2},{1,3},{2,0},{3,1},{4,6},{5,7},{6,4},{7,5},{8,10},{9,11},{10,... | collective-permute-start | bytes 196616 | tf_op jit(solution)/shard_map/ppermute | solution.py:33
  51.5 3.8 %collective-permute-start.25 = (f32[64,256]{1,0:T(8,128)S(1)}, f32[64,256]{1,0:T(8,128)S(1)}, u32[]{:S(2)}, u32[]{:S(2)}) collective-permute-start(f32[64,256]{1,0:T(8,128)S(1)} %get-tuple-element.62), channel_id=1, source_target_pairs={{0,2},{1,3},{2,0},{3,1},{4,6},{5,7},{6,4},{7,5},{8,10},{9,11},{10,... | collective-permute-start | bytes 196616 | tf_op jit(solution)/shard_map/ppermute | solution.py:33
  55.8 0.7 collective-permute-start.22
  57.0 0.6 constant_dynamic-update-slice_fusion.27
  57.7 2.8 %collective-permute-start.28 = (f32[64,256]{1,0:T(8,128)S(1)}, f32[64,256]{1,0:T(8,128)S(1)}, u32[]{:S(2)}, u32[]{:S(2)}) collective-permute-start(f32[64,256]{1,0:T(8,128)S(1)} %get-tuple-element.64), channel_id=1, source_target_pairs={{0,2},{1,3},{2,0},{3,1},{4,6},{5,7},{6,4},{7,5},{8,10},{9,11},{10,... | collective-permute-start | bytes 196616 | tf_op jit(solution)/shard_map/ppermute | solution.py:33
  60.5 1.2 collective-permute-start.29
  62.4 3.2 %collective-permute-start.31 = (f32[64,256]{1,0:T(8,128)S(1)}, f32[64,256]{1,0:T(8,128)S(1)}, u32[]{:S(2)}, u32[]{:S(2)}) collective-permute-start(f32[64,256]{1,0:T(8,128)S(1)} %get-tuple-element.66.refs_4_), channel_id=1, source_target_pairs={{0,2},{1,3},{2,0},{3,1},{4,6},{5,7},{6,4},{7,5},{8,10},{9,11},{10,... | collective-permute-start | bytes 196616 | tf_op jit(solution)/shard_map/ppermute | solution.py:33
  65.7 2.1 %collective-permute-start.32 = (f32[64,256]{1,0:T(8,128)S(1)}, f32[64,256]{1,0:T(8,128)S(1)}, u32[]{:S(2)}, u32[]{:S(2)}) collective-permute-start(f32[64,256]{1,0:T(8,128)S(1)} %get-tuple-element.66.refs_4_), channel_id=1, source_target_pairs={{0,3},{1,2},{2,1},{3,0},{4,7},{5,6},{6,5},{7,4},{8,11},{9,10},{10,... | collective-permute-start | bytes 196616 | tf_op jit(solution)/shard_map/ppermute | solution.py:33
  67.9 0.6 constant_dynamic-update-slice_fusion.18
  68.5 2.9 %collective-permute-start.35 = (f32[64,256]{1,0:T(8,128)S(1)}, f32[64,256]{1,0:T(8,128)S(1)}, u32[]{:S(2)}, u32[]{:S(2)}) collective-permute-start(f32[64,256]{1,0:T(8,128)S(1)} %get-tuple-element.68.refs_5_), channel_id=1, source_target_pairs={{0,2},{1,3},{2,0},{3,1},{4,6},{5,7},{6,4},{7,5},{8,10},{9,11},{10,... | collective-permute-start | bytes 196616 | tf_op jit(solution)/shard_map/ppermute | solution.py:33
  71.4 1.5 %collective-permute-start.36 = (f32[64,256]{1,0:T(8,128)S(1)}, f32[64,256]{1,0:T(8,128)S(1)}, u32[]{:S(2)}, u32[]{:S(2)}) collective-permute-start(f32[64,256]{1,0:T(8,128)S(1)} %get-tuple-element.68.refs_5_), channel_id=1, source_target_pairs={{0,3},{1,2},{2,1},{3,0},{4,7},{5,6},{6,5},{7,4},{8,11},{9,10},{10,... | collective-permute-start | bytes 196616 | tf_op jit(solution)/shard_map/ppermute | solution.py:33
  73.0 1.4 %collective-permute-done.30 = f32[64,256]{1,0:T(8,128)S(1)} collective-permute-done((f32[64,256]{1,0:T(8,128)S(1)}, f32[64,256]{1,0:T(8,128)S(1)}, u32[]{:S(2)}, u32[]{:S(2)}) %collective-permute-start.30) | collective-permute-done | bytes 65568 | tf_op jit(solution)/shard_map/ppermute | solution.py:33
  75.1 2.4 %collective-permute-start.37 = (f32[64,256]{1,0:T(8,128)S(1)}, f32[64,256]{1,0:T(8,128)S(1)}, u32[]{:S(2)}, u32[]{:S(2)}) collective-permute-start(f32[64,256]{1,0:T(8,128)S(1)} %get-tuple-element.70), channel_id=1, source_target_pairs={{0,2},{1,3},{2,0},{3,1},{4,6},{5,7},{6,4},{7,5},{8,10},{9,11},{10,... | collective-permute-start | bytes 196616 | tf_op jit(solution)/shard_map/ppermute | solution.py:33
  77.5 2.0 %collective-permute-start.38 = (f32[64,256]{1,0:T(8,128)S(1)}, f32[64,256]{1,0:T(8,128)S(1)}, u32[]{:S(2)}, u32[]{:S(2)}) collective-permute-start(f32[64,256]{1,0:T(8,128)S(1)} %get-tuple-element.70), channel_id=1, source_target_pairs={{0,3},{1,2},{2,1},{3,0},{4,7},{5,6},{6,5},{7,4},{8,11},{9,10},{10,... | collective-permute-start | bytes 196616 | tf_op jit(solution)/shard_map/ppermute | solution.py:33
  79.6 0.6 constant_dynamic-update-slice_fusion.11
  80.3 2.4 %collective-permute-start.40 = (f32[64,256]{1,0:T(8,128)S(1)}, f32[64,256]{1,0:T(8,128)S(1)}, u32[]{:S(2)}, u32[]{:S(2)}) collective-permute-start(f32[64,256]{1,0:T(8,128)S(1)} %get-tuple-element.72), channel_id=1, source_target_pairs={{0,2},{1,3},{2,0},{3,1},{4,6},{5,7},{6,4},{7,5},{8,10},{9,11},{10,... | collective-permute-start | bytes 196616 | tf_op jit(solution)/shard_map/ppermute | solution.py:33
  82.7 2.0 %collective-permute-start.41 = (f32[64,256]{1,0:T(8,128)S(1)}, f32[64,256]{1,0:T(8,128)S(1)}, u32[]{:S(2)}, u32[]{:S(2)}) collective-permute-start(f32[64,256]{1,0:T(8,128)S(1)} %get-tuple-element.72), channel_id=1, source_target_pairs={{0,3},{1,2},{2,1},{3,0},{4,7},{5,6},{6,5},{7,4},{8,11},{9,10},{10,... | collective-permute-start | bytes 196616 | tf_op jit(solution)/shard_map/ppermute | solution.py:33
  84.7 1.1 collective-permute-done.34
  86.0 0.6 constant_dynamic-update-slice_fusion.7
  86.7 1.4 %collective-permute-start.43 = (f32[64,256]{1,0:T(8,128)S(1)}, f32[64,256]{1,0:T(8,128)S(1)}, u32[]{:S(2)}, u32[]{:S(2)}) collective-permute-start(f32[64,256]{1,0:T(8,128)S(1)} %get-tuple-element.74.refs_6_), channel_id=1, source_target_pairs={{0,2},{1,3},{2,0},{3,1},{4,6},{5,7},{6,4},{7,5},{8,10},{9,11},{10,... | collective-permute-start | bytes 196616 | tf_op jit(solution)/shard_map/ppermute | solution.py:33
  88.1 2.9 %collective-permute-start.44 = (f32[64,256]{1,0:T(8,128)S(1)}, f32[64,256]{1,0:T(8,128)S(1)}, u32[]{:S(2)}, u32[]{:S(2)}) collective-permute-start(f32[64,256]{1,0:T(8,128)S(1)} %get-tuple-element.74.refs_6_), channel_id=1, source_target_pairs={{0,3},{1,2},{2,1},{3,0},{4,7},{5,6},{6,5},{7,4},{8,11},{9,10},{10,... | collective-permute-start | bytes 196616 | tf_op jit(solution)/shard_map/ppermute | solution.py:33
  91.0 1.6 %collective-permute-done.39 = f32[64,256]{1,0:T(8,128)S(1)} collective-permute-done((f32[64,256]{1,0:T(8,128)S(1)}, f32[64,256]{1,0:T(8,128)S(1)}, u32[]{:S(2)}, u32[]{:S(2)}) %collective-permute-start.39) | collective-permute-done | bytes 65568 | tf_op jit(solution)/shard_map/ppermute | solution.py:33
  93.9 3.9 %collective-permute-start.47 = (f32[64,256]{1,0:T(8,128)S(1)}, f32[64,256]{1,0:T(8,128)S(1)}, u32[]{:S(2)}, u32[]{:S(2)}) collective-permute-start(f32[64,256]{1,0:T(8,128)S(1)} %get-tuple-element.76.refs_7_), channel_id=1, source_target_pairs={{0,3},{1,2},{2,1},{3,0},{4,7},{5,6},{6,5},{7,4},{8,11},{9,10},{10,... | collective-permute-start | bytes 196616 | tf_op jit(solution)/shard_map/ppermute | solution.py:33
  97.9 1.2 shard_map.117.refs_0_
  99.1 2.9 %collective-permute-done.45 = f32[64,256]{1,0:T(8,128)S(1)} collective-permute-done((f32[64,256]{1,0:T(8,128)S(1)}, f32[64,256]{1,0:T(8,128)S(1)}, u32[]{:S(2)}, u32[]{:S(2)}) %collective-permute-start.45) | collective-permute-done | bytes 65568 | tf_op jit(solution)/shard_map/ppermute | solution.py:33
  102.1 1.2 shard_map.118
  103.4 1.3 collective-permute-done.48.refs_1_
  104.8 2.5 %collective-permute-start.49 = (f32[2,16,512]{2,1,0:T(8,128)S(1)}, f32[2,16,512]{2,1,0:T(8,128)S(1)}, u32[]{:S(2)}, u32[]{:S(2)}) collective-permute-start(f32[2,16,512]{2,1,0:T(8,128)S(1)} %get-tuple-element.82), channel_id=1, source_target_pairs={{0,24},{4,28},{8,16},{12,20},{16,8},{20,12},{24,0},{28,4},{1,25},{... | collective-permute-start | bytes 196616 | tf_op jit(solution)/shard_map/ppermute | solution.py:81
  108.3 1.0 shard_map.119
  109.3 0.7 collective-permute-done.49.refs_1_
  110.0 1.5 %collective-permute-done.50.refs_2_ = f32[2,16,512]{2,1,0:T(8,128)S(1)} collective-permute-done((f32[2,16,512]{2,1,0:T(8,128)S(1)}, f32[2,16,512]{2,1,0:T(8,128)S(1)}, u32[]{:S(2)}, u32[]{:S(2)}) %collective-permute-start.50) | collective-permute-done | bytes 65568 | tf_op jit(solution)/shard_map/ppermute | solution.py:81
  112.6 3.0 %collective-permute-start.53 = (f32[16,1280]{1,0:T(8,128)S(1)}, f32[16,1280]{1,0:T(8,128)S(1)}, u32[]{:S(2)}, u32[]{:S(2)}) collective-permute-start(f32[16,1280]{1,0:T(8,128)S(1)} %get-tuple-element.88), channel_id=1, source_target_pairs={{0,3},{1,2},{2,1},{3,0},{4,7},{5,6},{6,5},{7,4},{8,11},{9,10},{10,... | collective-permute-start | bytes 245768 | tf_op jit(solution)/shard_map/ppermute | solution.py:33
  116.5 4.1 %collective-permute-done.52.refs_1_ = f32[16,1280]{1,0:T(8,128)S(1)} collective-permute-done((f32[16,1280]{1,0:T(8,128)S(1)}, f32[16,1280]{1,0:T(8,128)S(1)}, u32[]{:S(2)}, u32[]{:S(2)}) %collective-permute-start.52) | collective-permute-done | bytes 81952 | tf_op jit(solution)/shard_map/ppermute | solution.py:33
  121.2 1.1 collective-permute-start.55
  122.3 2.6 %collective-permute-start.56 = (f32[16,256]{1,0:T(8,128)S(1)}, f32[16,256]{1,0:T(8,128)S(1)}, u32[]{:S(2)}, u32[]{:S(2)}) collective-permute-start(f32[16,256]{1,0:T(8,128)S(1)} %get-tuple-element.92.refs_0_.refs_6_), channel_id=1, source_target_pairs={{0,3},{1,2},{2,1},{3,0},{4,7},{5,6},{6,5},{7,4},{8,11},{9,10},{10,... | collective-permute-start | bytes 49160 | tf_op jit(solution)/shard_map/ppermute | solution.py:33
  124.9 0.9 collective-permute-done.55.refs_1_
  125.8 2.0 %collective-permute-done.56.refs_2_ = f32[16,256]{1,0:T(8,128)S(1)} collective-permute-done((f32[16,256]{1,0:T(8,128)S(1)}, f32[16,256]{1,0:T(8,128)S(1)}, u32[]{:S(2)}, u32[]{:S(2)}) %collective-permute-start.56) | collective-permute-done | bytes 16416 | tf_op jit(solution)/shard_map/ppermute | solution.py:33
  127.8 0.8 collective-permute-done.57.refs_3_
  129.1 2.5 %collective-permute-start.59 = (f32[16,256]{1,0:T(8,128)S(1)}, f32[16,256]{1,0:T(8,128)S(1)}, u32[]{:S(2)}, u32[]{:S(2)}) collective-permute-start(f32[16,256]{1,0:T(8,128)S(1)} %shard_map.124.refs_0_), channel_id=1, source_target_pairs={{0,3},{1,2},{2,1},{3,0},{4,7},{5,6},{6,5},{7,4},{8,11},{9,10},{10,... | collective-permute-start | bytes 49160 | tf_op jit(solution)/shard_map/ppermute | solution.py:33
  131.6 1.0 collective-permute-start.60
  132.5 1.1 collective-permute-done.58.refs_1_
  133.7 1.1 collective-permute-done.59.refs_2_
  135.3 1.0 shard_map.125
  (162 shorter events, 14.5 us)
Async XLA Ops:
  1.7 23.7 %copy-start.3 = (f32[1,4,256,128]{3,2,1,0:T(8,128)S(1)}, f32[1,4,256,128]{3,2,1,0:T(8,128)}, u32[]{:S(2)}) copy-start(f32[1,4,256,128]{3,2,1,0:T(8,128)} %rhs_ref.3) | copy-start | bytes 1572868
  1.9 10.1 %collective-permute-start = (f32[64,256]{1,0:T(8,128)S(1)}, f32[64,256]{1,0:T(8,128)S(1)}, u32[]{:S(2)}, u32[]{:S(2)}) collective-permute-start(f32[64,256]{1,0:T(8,128)S(1)} %get-tuple-element.49.refs_0_), channel_id=1, source_target_pairs={{0,1},{1,0},{2,3},{3,2},{4,5},{5,4},{6,7},{7,6},{8,9},{9,8},{10,11... | collective-permute-start | bytes 196616 | tf_op jit(solution)/shard_map/ppermute | solution.py:33
  5.0 9.1 %collective-permute-start.1 = (f32[64,256]{1,0:T(8,128)S(1)}, f32[64,256]{1,0:T(8,128)S(1)}, u32[]{:S(2)}, u32[]{:S(2)}) collective-permute-start(f32[64,256]{1,0:T(8,128)S(1)} %get-tuple-element.49.refs_0_), channel_id=1, source_target_pairs={{0,2},{1,3},{2,0},{3,1},{4,6},{5,7},{6,4},{7,5},{8,10},{9,11},{10,... | collective-permute-start | bytes 196616 | tf_op jit(solution)/shard_map/ppermute | solution.py:33
  7.6 6.6 %collective-permute-start.2 = (f32[64,256]{1,0:T(8,128)S(1)}, f32[64,256]{1,0:T(8,128)S(1)}, u32[]{:S(2)}, u32[]{:S(2)}) collective-permute-start(f32[64,256]{1,0:T(8,128)S(1)} %get-tuple-element.49.refs_0_), channel_id=1, source_target_pairs={{0,3},{1,2},{2,1},{3,0},{4,7},{5,6},{6,5},{7,4},{8,11},{9,10},{10,... | collective-permute-start | bytes 196616 | tf_op jit(solution)/shard_map/ppermute | solution.py:33
  7.6 12.2 %collective-permute-start.3 = (f32[64,256]{1,0:T(8,128)S(1)}, f32[64,256]{1,0:T(8,128)S(1)}, u32[]{:S(2)}, u32[]{:S(2)}) collective-permute-start(f32[64,256]{1,0:T(8,128)S(1)} %get-tuple-element.50.refs_0_), channel_id=1, source_target_pairs={{0,1},{1,0},{2,3},{3,2},{4,5},{5,4},{6,7},{7,6},{8,9},{9,8},{10,11... | collective-permute-start | bytes 196616 | tf_op jit(solution)/shard_map/ppermute | solution.py:33
  8.5 12.7 %collective-permute-start.4 = (f32[64,256]{1,0:T(8,128)S(1)}, f32[64,256]{1,0:T(8,128)S(1)}, u32[]{:S(2)}, u32[]{:S(2)}) collective-permute-start(f32[64,256]{1,0:T(8,128)S(1)} %get-tuple-element.50.refs_0_), channel_id=1, source_target_pairs={{0,2},{1,3},{2,0},{3,1},{4,6},{5,7},{6,4},{7,5},{8,10},{9,11},{10,... | collective-permute-start | bytes 196616 | tf_op jit(solution)/shard_map/ppermute | solution.py:33
  12.0 9.2 %collective-permute-start.5 = (f32[64,256]{1,0:T(8,128)S(1)}, f32[64,256]{1,0:T(8,128)S(1)}, u32[]{:S(2)}, u32[]{:S(2)}) collective-permute-start(f32[64,256]{1,0:T(8,128)S(1)} %get-tuple-element.50.refs_0_), channel_id=1, source_target_pairs={{0,3},{1,2},{2,1},{3,0},{4,7},{5,6},{6,5},{7,4},{8,11},{9,10},{10,... | collective-permute-start | bytes 196616 | tf_op jit(solution)/shard_map/ppermute | solution.py:33
  14.6 10.1 %collective-permute-start.6 = (f32[64,256]{1,0:T(8,128)S(1)}, f32[64,256]{1,0:T(8,128)S(1)}, u32[]{:S(2)}, u32[]{:S(2)}) collective-permute-start(f32[64,256]{1,0:T(8,128)S(1)} %shard_map.114.refs_0_), channel_id=1, source_target_pairs={{0,1},{1,0},{2,3},{3,2},{4,5},{5,4},{6,7},{7,6},{8,9},{9,8},{10,11... | collective-permute-start | bytes 196616 | tf_op jit(solution)/shard_map/ppermute | solution.py:33
  17.7 10.2 %collective-permute-start.7 = (f32[64,256]{1,0:T(8,128)S(1)}, f32[64,256]{1,0:T(8,128)S(1)}, u32[]{:S(2)}, u32[]{:S(2)}) collective-permute-start(f32[64,256]{1,0:T(8,128)S(1)} %shard_map.114.refs_0_), channel_id=1, source_target_pairs={{0,2},{1,3},{2,0},{3,1},{4,6},{5,7},{6,4},{7,5},{8,10},{9,11},{10,... | collective-permute-start | bytes 196616 | tf_op jit(solution)/shard_map/ppermute | solution.py:33
  19.8 8.1 %collective-permute-start.8 = (f32[64,256]{1,0:T(8,128)S(1)}, f32[64,256]{1,0:T(8,128)S(1)}, u32[]{:S(2)}, u32[]{:S(2)}) collective-permute-start(f32[64,256]{1,0:T(8,128)S(1)} %shard_map.114.refs_0_), channel_id=1, source_target_pairs={{0,3},{1,2},{2,1},{3,0},{4,7},{5,6},{6,5},{7,4},{8,11},{9,10},{10,... | collective-permute-start | bytes 196616 | tf_op jit(solution)/shard_map/ppermute | solution.py:33
  21.7 11.9 %collective-permute-start.11 = (f32[64,256]{1,0:T(8,128)S(1)}, f32[64,256]{1,0:T(8,128)S(1)}, u32[]{:S(2)}, u32[]{:S(2)}) collective-permute-start(f32[64,256]{1,0:T(8,128)S(1)} %shard_map.115.refs_1_), channel_id=1, source_target_pairs={{0,2},{1,3},{2,0},{3,1},{4,6},{5,7},{6,4},{7,5},{8,10},{9,11},{10,... | collective-permute-start | bytes 196616 | tf_op jit(solution)/shard_map/ppermute | solution.py:33
  24.0 9.6 %collective-permute-start.12 = (f32[64,256]{1,0:T(8,128)S(1)}, f32[64,256]{1,0:T(8,128)S(1)}, u32[]{:S(2)}, u32[]{:S(2)}) collective-permute-start(f32[64,256]{1,0:T(8,128)S(1)} %shard_map.115.refs_1_), channel_id=1, source_target_pairs={{0,3},{1,2},{2,1},{3,0},{4,7},{5,6},{6,5},{7,4},{8,11},{9,10},{10,... | collective-permute-start | bytes 196616 | tf_op jit(solution)/shard_map/ppermute | solution.py:33
  24.8 8.2 %collective-permute-start.9 = (f32[64,256]{1,0:T(8,128)S(1)}, f32[64,256]{1,0:T(8,128)S(1)}, u32[]{:S(2)}, u32[]{:S(2)}) collective-permute-start(f32[64,256]{1,0:T(8,128)S(1)} %shard_map.115.refs_1_), channel_id=1, source_target_pairs={{0,1},{1,0},{2,3},{3,2},{4,5},{5,4},{6,7},{7,6},{8,9},{9,8},{10,11... | collective-permute-start | bytes 196616 | tf_op jit(solution)/shard_map/ppermute | solution.py:33
  28.6 11.2 %collective-permute-start.13 = (f32[64,256]{1,0:T(8,128)S(1)}, f32[64,256]{1,0:T(8,128)S(1)}, u32[]{:S(2)}, u32[]{:S(2)}) collective-permute-start(f32[64,256]{1,0:T(8,128)S(1)} %get-tuple-element.54), channel_id=1, source_target_pairs={{0,2},{1,3},{2,0},{3,1},{4,6},{5,7},{6,4},{7,5},{8,10},{9,11},{10,... | collective-permute-start | bytes 196616 | tf_op jit(solution)/shard_map/ppermute | solution.py:33
  32.9 7.0 %collective-permute-start.14 = (f32[64,256]{1,0:T(8,128)S(1)}, f32[64,256]{1,0:T(8,128)S(1)}, u32[]{:S(2)}, u32[]{:S(2)}) collective-permute-start(f32[64,256]{1,0:T(8,128)S(1)} %get-tuple-element.54), channel_id=1, source_target_pairs={{0,3},{1,2},{2,1},{3,0},{4,7},{5,6},{6,5},{7,4},{8,11},{9,10},{10,... | collective-permute-start | bytes 196616 | tf_op jit(solution)/shard_map/ppermute | solution.py:33
  33.0 5.8 %collective-permute-start.10 = (f32[64,256]{1,0:T(8,128)S(1)}, f32[64,256]{1,0:T(8,128)S(1)}, u32[]{:S(2)}, u32[]{:S(2)}) collective-permute-start(f32[64,256]{1,0:T(8,128)S(1)} %get-tuple-element.54), channel_id=1, source_target_pairs={{0,1},{1,0},{2,3},{3,2},{4,5},{5,4},{6,7},{7,6},{8,9},{9,8},{10,11... | collective-permute-start | bytes 196616 | tf_op jit(solution)/shard_map/ppermute | solution.py:33
  34.2 10.3 %collective-permute-start.16 = (f32[64,256]{1,0:T(8,128)S(1)}, f32[64,256]{1,0:T(8,128)S(1)}, u32[]{:S(2)}, u32[]{:S(2)}) collective-permute-start(f32[64,256]{1,0:T(8,128)S(1)} %get-tuple-element.56), channel_id=1, source_target_pairs={{0,2},{1,3},{2,0},{3,1},{4,6},{5,7},{6,4},{7,5},{8,10},{9,11},{10,... | collective-permute-start | bytes 196616 | tf_op jit(solution)/shard_map/ppermute | solution.py:33
  38.0 6.6 %collective-permute-start.17 = (f32[64,256]{1,0:T(8,128)S(1)}, f32[64,256]{1,0:T(8,128)S(1)}, u32[]{:S(2)}, u32[]{:S(2)}) collective-permute-start(f32[64,256]{1,0:T(8,128)S(1)} %get-tuple-element.56), channel_id=1, source_target_pairs={{0,3},{1,2},{2,1},{3,0},{4,7},{5,6},{6,5},{7,4},{8,11},{9,10},{10,... | collective-permute-start | bytes 196616 | tf_op jit(solution)/shard_map/ppermute | solution.py:33
  38.7 5.2 %collective-permute-start.15 = (f32[64,256]{1,0:T(8,128)S(1)}, f32[64,256]{1,0:T(8,128)S(1)}, u32[]{:S(2)}, u32[]{:S(2)}) collective-permute-start(f32[64,256]{1,0:T(8,128)S(1)} %get-tuple-element.56), channel_id=1, source_target_pairs={{0,1},{1,0},{2,3},{3,2},{4,5},{5,4},{6,7},{7,6},{8,9},{9,8},{10,11... | collective-permute-start | bytes 196616 | tf_op jit(solution)/shard_map/ppermute | solution.py:33
  40.5 10.2 %collective-permute-start.19 = (f32[64,256]{1,0:T(8,128)S(1)}, f32[64,256]{1,0:T(8,128)S(1)}, u32[]{:S(2)}, u32[]{:S(2)}) collective-permute-start(f32[64,256]{1,0:T(8,128)S(1)} %get-tuple-element.58.refs_2_), channel_id=1, source_target_pairs={{0,2},{1,3},{2,0},{3,1},{4,6},{5,7},{6,4},{7,5},{8,10},{9,11},{10,... | collective-permute-start | bytes 196616 | tf_op jit(solution)/shard_map/ppermute | solution.py:33
  43.2 7.6 %collective-permute-start.20 = (f32[64,256]{1,0:T(8,128)S(1)}, f32[64,256]{1,0:T(8,128)S(1)}, u32[]{:S(2)}, u32[]{:S(2)}) collective-permute-start(f32[64,256]{1,0:T(8,128)S(1)} %get-tuple-element.58.refs_2_), channel_id=1, source_target_pairs={{0,3},{1,2},{2,1},{3,0},{4,7},{5,6},{6,5},{7,4},{8,11},{9,10},{10,... | collective-permute-start | bytes 196616 | tf_op jit(solution)/shard_map/ppermute | solution.py:33
  43.9 6.7 %collective-permute-start.18 = (f32[64,256]{1,0:T(8,128)S(1)}, f32[64,256]{1,0:T(8,128)S(1)}, u32[]{:S(2)}, u32[]{:S(2)}) collective-permute-start(f32[64,256]{1,0:T(8,128)S(1)} %get-tuple-element.58.refs_2_), channel_id=1, source_target_pairs={{0,1},{1,0},{2,3},{3,2},{4,5},{5,4},{6,7},{7,6},{8,9},{9,8},{10,11... | collective-permute-start | bytes 196616 | tf_op jit(solution)/shard_map/ppermute | solution.py:33
  45.3 11.2 %collective-permute-start.23 = (f32[64,256]{1,0:T(8,128)S(1)}, f32[64,256]{1,0:T(8,128)S(1)}, u32[]{:S(2)}, u32[]{:S(2)}) collective-permute-start(f32[64,256]{1,0:T(8,128)S(1)} %get-tuple-element.60.refs_3_), channel_id=1, source_target_pairs={{0,2},{1,3},{2,0},{3,1},{4,6},{5,7},{6,4},{7,5},{8,10},{9,11},{10,... | collective-permute-start | bytes 196616 | tf_op jit(solution)/shard_map/ppermute | solution.py:33
  50.1 6.9 %collective-permute-start.24 = (f32[64,256]{1,0:T(8,128)S(1)}, f32[64,256]{1,0:T(8,128)S(1)}, u32[]{:S(2)}, u32[]{:S(2)}) collective-permute-start(f32[64,256]{1,0:T(8,128)S(1)} %get-tuple-element.60.refs_3_), channel_id=1, source_target_pairs={{0,3},{1,2},{2,1},{3,0},{4,7},{5,6},{6,5},{7,4},{8,11},{9,10},{10,... | collective-permute-start | bytes 196616 | tf_op jit(solution)/shard_map/ppermute | solution.py:33
  50.6 5.2 %collective-permute-start.21 = (f32[64,256]{1,0:T(8,128)S(1)}, f32[64,256]{1,0:T(8,128)S(1)}, u32[]{:S(2)}, u32[]{:S(2)}) collective-permute-start(f32[64,256]{1,0:T(8,128)S(1)} %get-tuple-element.60.refs_3_), channel_id=1, source_target_pairs={{0,1},{1,0},{2,3},{3,2},{4,5},{5,4},{6,7},{7,6},{8,9},{9,8},{10,11... | collective-permute-start | bytes 196616 | tf_op jit(solution)/shard_map/ppermute | solution.py:33
  51.5 10.2 %collective-permute-start.25 = (f32[64,256]{1,0:T(8,128)S(1)}, f32[64,256]{1,0:T(8,128)S(1)}, u32[]{:S(2)}, u32[]{:S(2)}) collective-permute-start(f32[64,256]{1,0:T(8,128)S(1)} %get-tuple-element.62), channel_id=1, source_target_pairs={{0,2},{1,3},{2,0},{3,1},{4,6},{5,7},{6,4},{7,5},{8,10},{9,11},{10,... | collective-permute-start | bytes 196616 | tf_op jit(solution)/shard_map/ppermute | solution.py:33
  55.3 6.5 %collective-permute-start.26 = (f32[64,256]{1,0:T(8,128)S(1)}, f32[64,256]{1,0:T(8,128)S(1)}, u32[]{:S(2)}, u32[]{:S(2)}) collective-permute-start(f32[64,256]{1,0:T(8,128)S(1)} %get-tuple-element.62), channel_id=1, source_target_pairs={{0,3},{1,2},{2,1},{3,0},{4,7},{5,6},{6,5},{7,4},{8,11},{9,10},{10,... | collective-permute-start | bytes 196616 | tf_op jit(solution)/shard_map/ppermute | solution.py:33
  55.8 5.9 %collective-permute-start.22 = (f32[64,256]{1,0:T(8,128)S(1)}, f32[64,256]{1,0:T(8,128)S(1)}, u32[]{:S(2)}, u32[]{:S(2)}) collective-permute-start(f32[64,256]{1,0:T(8,128)S(1)} %get-tuple-element.62), channel_id=1, source_target_pairs={{0,1},{1,0},{2,3},{3,2},{4,5},{5,4},{6,7},{7,6},{8,9},{9,8},{10,11... | collective-permute-start | bytes 196616 | tf_op jit(solution)/shard_map/ppermute | solution.py:33
  57.7 10.1 %collective-permute-start.28 = (f32[64,256]{1,0:T(8,128)S(1)}, f32[64,256]{1,0:T(8,128)S(1)}, u32[]{:S(2)}, u32[]{:S(2)}) collective-permute-start(f32[64,256]{1,0:T(8,128)S(1)} %get-tuple-element.64), channel_id=1, source_target_pairs={{0,2},{1,3},{2,0},{3,1},{4,6},{5,7},{6,4},{7,5},{8,10},{9,11},{10,... | collective-permute-start | bytes 196616 | tf_op jit(solution)/shard_map/ppermute | solution.py:33
  60.5 7.4 %collective-permute-start.29 = (f32[64,256]{1,0:T(8,128)S(1)}, f32[64,256]{1,0:T(8,128)S(1)}, u32[]{:S(2)}, u32[]{:S(2)}) collective-permute-start(f32[64,256]{1,0:T(8,128)S(1)} %get-tuple-element.64), channel_id=1, source_target_pairs={{0,3},{1,2},{2,1},{3,0},{4,7},{5,6},{6,5},{7,4},{8,11},{9,10},{10,... | collective-permute-start | bytes 196616 | tf_op jit(solution)/shard_map/ppermute | solution.py:33
  61.7 6.1 %collective-permute-start.27 = (f32[64,256]{1,0:T(8,128)S(1)}, f32[64,256]{1,0:T(8,128)S(1)}, u32[]{:S(2)}, u32[]{:S(2)}) collective-permute-start(f32[64,256]{1,0:T(8,128)S(1)} %get-tuple-element.64), channel_id=1, source_target_pairs={{0,1},{1,0},{2,3},{3,2},{4,5},{5,4},{6,7},{7,6},{8,9},{9,8},{10,11... | collective-permute-start | bytes 196616 | tf_op jit(solution)/shard_map/ppermute | solution.py:33
  62.4 11.9 %collective-permute-start.31 = (f32[64,256]{1,0:T(8,128)S(1)}, f32[64,256]{1,0:T(8,128)S(1)}, u32[]{:S(2)}, u32[]{:S(2)}) collective-permute-start(f32[64,256]{1,0:T(8,128)S(1)} %get-tuple-element.66.refs_4_), channel_id=1, source_target_pairs={{0,2},{1,3},{2,0},{3,1},{4,6},{5,7},{6,4},{7,5},{8,10},{9,11},{10,... | collective-permute-start | bytes 196616 | tf_op jit(solution)/shard_map/ppermute | solution.py:33
  65.7 8.7 %collective-permute-start.32 = (f32[64,256]{1,0:T(8,128)S(1)}, f32[64,256]{1,0:T(8,128)S(1)}, u32[]{:S(2)}, u32[]{:S(2)}) collective-permute-start(f32[64,256]{1,0:T(8,128)S(1)} %get-tuple-element.66.refs_4_), channel_id=1, source_target_pairs={{0,3},{1,2},{2,1},{3,0},{4,7},{5,6},{6,5},{7,4},{8,11},{9,10},{10,... | collective-permute-start | bytes 196616 | tf_op jit(solution)/shard_map/ppermute | solution.py:33
  67.8 6.5 %collective-permute-start.30 = (f32[64,256]{1,0:T(8,128)S(1)}, f32[64,256]{1,0:T(8,128)S(1)}, u32[]{:S(2)}, u32[]{:S(2)}) collective-permute-start(f32[64,256]{1,0:T(8,128)S(1)} %get-tuple-element.66.refs_4_), channel_id=1, source_target_pairs={{0,1},{1,0},{2,3},{3,2},{4,5},{5,4},{6,7},{7,6},{8,9},{9,8},{10,11... | collective-permute-start | bytes 196616 | tf_op jit(solution)/shard_map/ppermute | solution.py:33
  68.5 11.0 %collective-permute-start.35 = (f32[64,256]{1,0:T(8,128)S(1)}, f32[64,256]{1,0:T(8,128)S(1)}, u32[]{:S(2)}, u32[]{:S(2)}) collective-permute-start(f32[64,256]{1,0:T(8,128)S(1)} %get-tuple-element.68.refs_5_), channel_id=1, source_target_pairs={{0,2},{1,3},{2,0},{3,1},{4,6},{5,7},{6,4},{7,5},{8,10},{9,11},{10,... | collective-permute-start | bytes 196616 | tf_op jit(solution)/shard_map/ppermute | solution.py:33
  71.4 8.1 %collective-permute-start.36 = (f32[64,256]{1,0:T(8,128)S(1)}, f32[64,256]{1,0:T(8,128)S(1)}, u32[]{:S(2)}, u32[]{:S(2)}) collective-permute-start(f32[64,256]{1,0:T(8,128)S(1)} %get-tuple-element.68.refs_5_), channel_id=1, source_target_pairs={{0,3},{1,2},{2,1},{3,0},{4,7},{5,6},{6,5},{7,4},{8,11},{9,10},{10,... | collective-permute-start | bytes 196616 | tf_op jit(solution)/shard_map/ppermute | solution.py:33
  74.3 5.2 %collective-permute-start.33 = (f32[64,256]{1,0:T(8,128)S(1)}, f32[64,256]{1,0:T(8,128)S(1)}, u32[]{:S(2)}, u32[]{:S(2)}) collective-permute-start(f32[64,256]{1,0:T(8,128)S(1)} %get-tuple-element.68.refs_5_), channel_id=1, source_target_pairs={{0,1},{1,0},{2,3},{3,2},{4,5},{5,4},{6,7},{7,6},{8,9},{9,8},{10,11... | collective-permute-start | bytes 196616 | tf_op jit(solution)/shard_map/ppermute | solution.py:33
  75.1 10.9 %collective-permute-start.37 = (f32[64,256]{1,0:T(8,128)S(1)}, f32[64,256]{1,0:T(8,128)S(1)}, u32[]{:S(2)}, u32[]{:S(2)}) collective-permute-start(f32[64,256]{1,0:T(8,128)S(1)} %get-tuple-element.70), channel_id=1, source_target_pairs={{0,2},{1,3},{2,0},{3,1},{4,6},{5,7},{6,4},{7,5},{8,10},{9,11},{10,... | collective-permute-start | bytes 196616 | tf_op jit(solution)/shard_map/ppermute | solution.py:33
  77.5 8.5 %collective-permute-start.38 = (f32[64,256]{1,0:T(8,128)S(1)}, f32[64,256]{1,0:T(8,128)S(1)}, u32[]{:S(2)}, u32[]{:S(2)}) collective-permute-start(f32[64,256]{1,0:T(8,128)S(1)} %get-tuple-element.70), channel_id=1, source_target_pairs={{0,3},{1,2},{2,1},{3,0},{4,7},{5,6},{6,5},{7,4},{8,11},{9,10},{10,... | collective-permute-start | bytes 196616 | tf_op jit(solution)/shard_map/ppermute | solution.py:33
  79.5 6.3 %collective-permute-start.34 = (f32[64,256]{1,0:T(8,128)S(1)}, f32[64,256]{1,0:T(8,128)S(1)}, u32[]{:S(2)}, u32[]{:S(2)}) collective-permute-start(f32[64,256]{1,0:T(8,128)S(1)} %get-tuple-element.70), channel_id=1, source_target_pairs={{0,1},{1,0},{2,3},{3,2},{4,5},{5,4},{6,7},{7,6},{8,9},{9,8},{10,11... | collective-permute-start | bytes 196616 | tf_op jit(solution)/shard_map/ppermute | solution.py:33
  79.6 18.3 %copy-start = (f32[1,1,3,128,1024]{4,3,2,1,0:T(8,128)S(1)}, f32[1,1,3,128,1024]{4,3,2,1,0:T(8,128)}, u32[]{:S(2)}) copy-start(f32[1,1,3,128,1024]{4,3,2,1,0:T(8,128)} %param.13) | copy-start | bytes 4718596
  79.6 18.3 %copy-start.6 = (s32[1,1,3]{2,1,0:T(1,128)S(1)}, s32[1,1,3]{2,1,0:T(1,128)}, u32[]{:S(2)}) copy-start(s32[1,1,3]{2,1,0:T(1,128)} %refs_6_.1) | copy-start | bytes 40
  80.3 12.3 %collective-permute-start.40 = (f32[64,256]{1,0:T(8,128)S(1)}, f32[64,256]{1,0:T(8,128)S(1)}, u32[]{:S(2)}, u32[]{:S(2)}) collective-permute-start(f32[64,256]{1,0:T(8,128)S(1)} %get-tuple-element.72), channel_id=1, source_target_pairs={{0,2},{1,3},{2,0},{3,1},{4,6},{5,7},{6,4},{7,5},{8,10},{9,11},{10,... | collective-permute-start | bytes 196616 | tf_op jit(solution)/shard_map/ppermute | solution.py:33
  82.7 10.0 %collective-permute-start.41 = (f32[64,256]{1,0:T(8,128)S(1)}, f32[64,256]{1,0:T(8,128)S(1)}, u32[]{:S(2)}, u32[]{:S(2)}) collective-permute-start(f32[64,256]{1,0:T(8,128)S(1)} %get-tuple-element.72), channel_id=1, source_target_pairs={{0,3},{1,2},{2,1},{3,0},{4,7},{5,6},{6,5},{7,4},{8,11},{9,10},{10,... | collective-permute-start | bytes 196616 | tf_op jit(solution)/shard_map/ppermute | solution.py:33
  85.8 6.8 %collective-permute-start.39 = (f32[64,256]{1,0:T(8,128)S(1)}, f32[64,256]{1,0:T(8,128)S(1)}, u32[]{:S(2)}, u32[]{:S(2)}) collective-permute-start(f32[64,256]{1,0:T(8,128)S(1)} %get-tuple-element.72), channel_id=1, source_target_pairs={{0,1},{1,0},{2,3},{3,2},{4,5},{5,4},{6,7},{7,6},{8,9},{9,8},{10,11... | collective-permute-start | bytes 196616 | tf_op jit(solution)/shard_map/ppermute | solution.py:33
  86.7 11.1 %collective-permute-start.43 = (f32[64,256]{1,0:T(8,128)S(1)}, f32[64,256]{1,0:T(8,128)S(1)}, u32[]{:S(2)}, u32[]{:S(2)}) collective-permute-start(f32[64,256]{1,0:T(8,128)S(1)} %get-tuple-element.74.refs_6_), channel_id=1, source_target_pairs={{0,2},{1,3},{2,0},{3,1},{4,6},{5,7},{6,4},{7,5},{8,10},{9,11},{10,... | collective-permute-start | bytes 196616 | tf_op jit(solution)/shard_map/ppermute | solution.py:33
  88.1 9.7 %collective-permute-start.44 = (f32[64,256]{1,0:T(8,128)S(1)}, f32[64,256]{1,0:T(8,128)S(1)}, u32[]{:S(2)}, u32[]{:S(2)}) collective-permute-start(f32[64,256]{1,0:T(8,128)S(1)} %get-tuple-element.74.refs_6_), channel_id=1, source_target_pairs={{0,3},{1,2},{2,1},{3,0},{4,7},{5,6},{6,5},{7,4},{8,11},{9,10},{10,... | collective-permute-start | bytes 196616 | tf_op jit(solution)/shard_map/ppermute | solution.py:33
  92.6 5.2 %collective-permute-start.42 = (f32[64,256]{1,0:T(8,128)S(1)}, f32[64,256]{1,0:T(8,128)S(1)}, u32[]{:S(2)}, u32[]{:S(2)}) collective-permute-start(f32[64,256]{1,0:T(8,128)S(1)} %get-tuple-element.74.refs_6_), channel_id=1, source_target_pairs={{0,1},{1,0},{2,3},{3,2},{4,5},{5,4},{6,7},{7,6},{8,9},{9,8},{10,11... | collective-permute-start | bytes 196616 | tf_op jit(solution)/shard_map/ppermute | solution.py:33
  93.3 8.7 %collective-permute-start.46 = (f32[64,256]{1,0:T(8,128)S(1)}, f32[64,256]{1,0:T(8,128)S(1)}, u32[]{:S(2)}, u32[]{:S(2)}) collective-permute-start(f32[64,256]{1,0:T(8,128)S(1)} %get-tuple-element.76.refs_7_), channel_id=1, source_target_pairs={{0,2},{1,3},{2,0},{3,1},{4,6},{5,7},{6,4},{7,5},{8,10},{9,11},{10,... | collective-permute-start | bytes 196616 | tf_op jit(solution)/shard_map/ppermute | solution.py:33
  93.9 8.2 %collective-permute-start.47 = (f32[64,256]{1,0:T(8,128)S(1)}, f32[64,256]{1,0:T(8,128)S(1)}, u32[]{:S(2)}, u32[]{:S(2)}) collective-permute-start(f32[64,256]{1,0:T(8,128)S(1)} %get-tuple-element.76.refs_7_), channel_id=1, source_target_pairs={{0,3},{1,2},{2,1},{3,0},{4,7},{5,6},{6,5},{7,4},{8,11},{9,10},{10,... | collective-permute-start | bytes 196616 | tf_op jit(solution)/shard_map/ppermute | solution.py:33
  97.8 4.3 %collective-permute-start.45 = (f32[64,256]{1,0:T(8,128)S(1)}, f32[64,256]{1,0:T(8,128)S(1)}, u32[]{:S(2)}, u32[]{:S(2)}) collective-permute-start(f32[64,256]{1,0:T(8,128)S(1)} %get-tuple-element.76.refs_7_), channel_id=1, source_target_pairs={{0,1},{1,0},{2,3},{3,2},{4,5},{5,4},{6,7},{7,6},{8,9},{9,8},{10,11... | collective-permute-start | bytes 196616 | tf_op jit(solution)/shard_map/ppermute | solution.py:33
  103.3 1.4 %collective-permute-start.48 = (f32[4,16,512]{2,1,0:T(8,128)S(1)}, f32[4,16,512]{2,1,0:T(8,128)S(1)}, u32[]{:S(2)}, u32[]{:S(2)}) collective-permute-start(f32[4,16,512]{2,1,0:T(8,128)S(1)} %get-tuple-element.80), channel_id=1, source_target_pairs={{0,4},{4,0},{8,12},{12,8},{16,20},{20,16},{24,28},{28,24},{1,5},{5... | collective-permute-start | bytes 393224 | tf_op jit(solution)/shard_map/ppermute | solution.py:281
  104.8 5.3 %collective-permute-start.49 = (f32[2,16,512]{2,1,0:T(8,128)S(1)}, f32[2,16,512]{2,1,0:T(8,128)S(1)}, u32[]{:S(2)}, u32[]{:S(2)}) collective-permute-start(f32[2,16,512]{2,1,0:T(8,128)S(1)} %get-tuple-element.82), channel_id=1, source_target_pairs={{0,24},{4,28},{8,16},{12,20},{16,8},{20,12},{24,0},{28,4},{1,25},{... | collective-permute-start | bytes 196616 | tf_op jit(solution)/shard_map/ppermute | solution.py:81
  107.3 4.3 %collective-permute-start.50 = (f32[2,16,512]{2,1,0:T(8,128)S(1)}, f32[2,16,512]{2,1,0:T(8,128)S(1)}, u32[]{:S(2)}, u32[]{:S(2)}) collective-permute-start(f32[2,16,512]{2,1,0:T(8,128)S(1)} %get-tuple-element.83), channel_id=1, source_target_pairs={{0,16},{4,20},{8,24},{12,28},{16,0},{20,4},{24,8},{28,12},{1,17},{... | collective-permute-start | bytes 196616 | tf_op jit(solution)/shard_map/ppermute | solution.py:81
  107.8 4.3 %collective-permute-start.51 = (f32[2,16,512]{2,1,0:T(8,128)S(1)}, f32[2,16,512]{2,1,0:T(8,128)S(1)}, u32[]{:S(2)}, u32[]{:S(2)}) collective-permute-start(f32[2,16,512]{2,1,0:T(8,128)S(1)} %get-tuple-element.84), channel_id=1, source_target_pairs={{0,8},{4,12},{8,0},{12,4},{16,24},{20,28},{24,16},{28,20},{1,9},{5... | collective-permute-start | bytes 196616 | tf_op jit(solution)/shard_map/ppermute | solution.py:81
  112.5 8.1 %collective-permute-start.52 = (f32[16,1280]{1,0:T(8,128)S(1)}, f32[16,1280]{1,0:T(8,128)S(1)}, u32[]{:S(2)}, u32[]{:S(2)}) collective-permute-start(f32[16,1280]{1,0:T(8,128)S(1)} %get-tuple-element.87), channel_id=1, source_target_pairs={{0,2},{1,3},{2,0},{3,1},{4,6},{5,7},{6,4},{7,5},{8,10},{9,11},{10,... | collective-permute-start | bytes 245768 | tf_op jit(solution)/shard_map/ppermute | solution.py:33
  112.6 8.0 %collective-permute-start.53 = (f32[16,1280]{1,0:T(8,128)S(1)}, f32[16,1280]{1,0:T(8,128)S(1)}, u32[]{:S(2)}, u32[]{:S(2)}) collective-permute-start(f32[16,1280]{1,0:T(8,128)S(1)} %get-tuple-element.88), channel_id=1, source_target_pairs={{0,3},{1,2},{2,1},{3,0},{4,7},{5,6},{6,5},{7,4},{8,11},{9,10},{10,... | collective-permute-start | bytes 245768 | tf_op jit(solution)/shard_map/ppermute | solution.py:33
  115.6 5.2 %collective-permute-start.54 = (f32[16,1280]{1,0:T(8,128)S(1)}, f32[16,1280]{1,0:T(8,128)S(1)}, u32[]{:S(2)}, u32[]{:S(2)}) collective-permute-start(f32[16,1280]{1,0:T(8,128)S(1)} %get-tuple-element.89), channel_id=1, source_target_pairs={{0,1},{1,0},{2,3},{3,2},{4,5},{5,4},{6,7},{7,6},{8,9},{9,8},{10,11... | collective-permute-start | bytes 245768 | tf_op jit(solution)/shard_map/ppermute | solution.py:33
  121.2 4.7 %collective-permute-start.55 = (f32[16,256]{1,0:T(8,128)S(1)}, f32[16,256]{1,0:T(8,128)S(1)}, u32[]{:S(2)}, u32[]{:S(2)}) collective-permute-start(f32[16,256]{1,0:T(8,128)S(1)} %get-tuple-element.92.refs_0_.refs_6_), channel_id=1, source_target_pairs={{0,2},{1,3},{2,0},{3,1},{4,6},{5,7},{6,4},{7,5},{8,10},{9,11},{10,... | collective-permute-start | bytes 49160 | tf_op jit(solution)/shard_map/ppermute | solution.py:33
  122.3 5.5 %collective-permute-start.56 = (f32[16,256]{1,0:T(8,128)S(1)}, f32[16,256]{1,0:T(8,128)S(1)}, u32[]{:S(2)}, u32[]{:S(2)}) collective-permute-start(f32[16,256]{1,0:T(8,128)S(1)} %get-tuple-element.92.refs_0_.refs_6_), channel_id=1, source_target_pairs={{0,3},{1,2},{2,1},{3,0},{4,7},{5,6},{6,5},{7,4},{8,11},{9,10},{10,... | collective-permute-start | bytes 49160 | tf_op jit(solution)/shard_map/ppermute | solution.py:33
  124.9 3.7 %collective-permute-start.57 = (f32[16,256]{1,0:T(8,128)S(1)}, f32[16,256]{1,0:T(8,128)S(1)}, u32[]{:S(2)}, u32[]{:S(2)}) collective-permute-start(f32[16,256]{1,0:T(8,128)S(1)} %get-tuple-element.92.refs_0_.refs_6_), channel_id=1, source_target_pairs={{0,1},{1,0},{2,3},{3,2},{4,5},{5,4},{6,7},{7,6},{8,9},{9,8},{10,11... | collective-permute-start | bytes 49160 | tf_op jit(solution)/shard_map/ppermute | solution.py:33
  129.0 4.7 %collective-permute-start.58 = (f32[16,256]{1,0:T(8,128)S(1)}, f32[16,256]{1,0:T(8,128)S(1)}, u32[]{:S(2)}, u32[]{:S(2)}) collective-permute-start(f32[16,256]{1,0:T(8,128)S(1)} %shard_map.124.refs_0_), channel_id=1, source_target_pairs={{0,2},{1,3},{2,0},{3,1},{4,6},{5,7},{6,4},{7,5},{8,10},{9,11},{10,... | collective-permute-start | bytes 49160 | tf_op jit(solution)/shard_map/ppermute | solution.py:33
  129.1 5.6 %collective-permute-start.59 = (f32[16,256]{1,0:T(8,128)S(1)}, f32[16,256]{1,0:T(8,128)S(1)}, u32[]{:S(2)}, u32[]{:S(2)}) collective-permute-start(f32[16,256]{1,0:T(8,128)S(1)} %shard_map.124.refs_0_), channel_id=1, source_target_pairs={{0,3},{1,2},{2,1},{3,0},{4,7},{5,6},{6,5},{7,4},{8,11},{9,10},{10,... | collective-permute-start | bytes 49160 | tf_op jit(solution)/shard_map/ppermute | solution.py:33
  131.6 3.7 %collective-permute-start.60 = (f32[16,256]{1,0:T(8,128)S(1)}, f32[16,256]{1,0:T(8,128)S(1)}, u32[]{:S(2)}, u32[]{:S(2)}) collective-permute-start(f32[16,256]{1,0:T(8,128)S(1)} %shard_map.124.refs_0_), channel_id=1, source_target_pairs={{0,1},{1,0},{2,3},{3,2},{4,5},{5,4},{6,7},{7,6},{8,9},{9,8},{10,11... | collective-permute-start | bytes 49160 | tf_op jit(solution)/shard_map/ppermute | solution.py:33
  (7 other events, 96.0 us)

commit v20 on v19

--- a/solution.py
+++ b/solution.py
@@ -460,13 +460,13 @@
         current = step // 2
         for i in range(streams):
             turn_taken = step > 0 and last is not None
-            ties = [(1, last[0][1][1])] if step * streams + i > streams else []
+            ties = [(1, last[0][2][1])] if step * streams + i > streams else []
             pieces = gather_rows(values[i], ties)
             if step == 1 and i == 0:
                 later = turn(rhs_local, 1, supernodes, streams, pieces[1][1])
             if turn_taken:
-                offset, piece = pieces[1]
-                pieces[1] = (offset, lax.optimization_barrier((piece, last[1]))[0])
+                offset, piece = pieces[2]
+                pieces[2] = (offset, lax.optimization_barrier((piece, last[1]))[0])
             if step == 0:
                 owned = apply_split(
                     [p for _, p in pieces],

time: 137 us -> 135 us (0.985)
  waiting for transfers between devices: 25.2 us -> 23.8 us
    ppermute x57, waiting for transfers between devices: 21.2 us -> 19.7 us  [send(): return lax.ppermute(value, axis, pairs)]
  transfers between devices with their start and end apart: 61 -> 61, of which waited for: 21 -> 17; matrix products, arithmetic and copies ran while one was open for 7% -> 7% of each run, Pallas kernels for 3% -> 3%
where the time goes in v20:
time: 135 us; the launch traced here: 134 us
  starting transfers between devices  90.2 us (67%)
  waiting for transfers between devices  23.8 us (18%)
  Pallas kernels  7.53 us (6%)
  matrix products  7.53 us (6%)
  between operations  2.07 us (2%)
  local copies, waits for them, and re-layouts  1.85 us (1%)
  other arithmetic  1.41 us (1%)
    ppermute x57, starting transfers between devices, send(): return lax.ppermute(value, axis, pairs)  86.6 us
    ppermute x57, waiting for transfers between devices, send(): return lax.ppermute(value, axis, pairs)  19.7 us
    dot_general x12, matrix products, contract_last(): lax.dot_general(left, right, (((left.ndim - 1,), (right.ndim - 1,)), ((),...  7.53 us
    pallas_call x13, Pallas kernels, local_kernel(): pl.pallas_call(body, out_shape=list(outs), in_specs=specs or [VMEM] * len...  7.53 us
    ppermute x3, starting transfers between devices, swap(): return lax.ppermute(value, axis, pairs)  3.55 us
    ppermute x3, waiting for transfers between devices, swap(): return lax.ppermute(value, axis, pairs)  2.74 us
  transfers between devices with their start and end apart: 61, of which 17 were waited for; matrix products, arithmetic and copies ran while one was open for 7% of the time, Pallas kernels for 3%

profile of v20, /device:TPU:0, one launch (start us, length us, event | category | flops | bytes accessed | tf_op | source)
XLA Modules:
  0.0 134.4 jit_solution(704805649007365102)
XLA Ops:
  0.6 1.0 copy-done.2
  1.9 3.1 %collective-permute-start = (f32[64,256]{1,0:T(8,128)S(1)}, f32[64,256]{1,0:T(8,128)S(1)}, u32[]{:S(2)}, u32[]{:S(2)}) collective-permute-start(f32[64,256]{1,0:T(8,128)S(1)} %get-tuple-element.49.refs_0_), channel_id=1, source_target_pairs={{0,1},{1,0},{2,3},{3,2},{4,5},{5,4},{6,7},{7,6},{8,9},{9,8},{10,11... | collective-permute-start | bytes 196616 | tf_op jit(solution)/shard_map/ppermute | solution.py:33
  5.0 2.6 %collective-permute-start.1 = (f32[64,256]{1,0:T(8,128)S(1)}, f32[64,256]{1,0:T(8,128)S(1)}, u32[]{:S(2)}, u32[]{:S(2)}) collective-permute-start(f32[64,256]{1,0:T(8,128)S(1)} %get-tuple-element.49.refs_0_), channel_id=1, source_target_pairs={{0,2},{1,3},{2,0},{3,1},{4,6},{5,7},{6,4},{7,5},{8,10},{9,11},{10,... | collective-permute-start | bytes 196616 | tf_op jit(solution)/shard_map/ppermute | solution.py:33
  7.6 0.9 collective-permute-start.3
  8.5 3.5 %collective-permute-start.4 = (f32[64,256]{1,0:T(8,128)S(1)}, f32[64,256]{1,0:T(8,128)S(1)}, u32[]{:S(2)}, u32[]{:S(2)}) collective-permute-start(f32[64,256]{1,0:T(8,128)S(1)} %get-tuple-element.50.refs_0_), channel_id=1, source_target_pairs={{0,2},{1,3},{2,0},{3,1},{4,6},{5,7},{6,4},{7,5},{8,10},{9,11},{10,... | collective-permute-start | bytes 196616 | tf_op jit(solution)/shard_map/ppermute | solution.py:33
  12.0 1.4 %fusion = (bf16[1,256,1024]{2,1,0:T(8,128)(2,1)S(1)}, bf16[1,256,1024]{2,1,0:T(8,128)(2,1)S(1)}) fusion(f32[1,4,256,1024]{3,2,1,0:T(8,128)} %param.11), kind=kLoop, calls=%fused_computation.2 | loop fusion | flops 1048576 | bytes 2097152 | tf_op jit(solution)/shard_map/convert_element_type | solution.py:454
  14.6 3.0 %collective-permute-start.6 = (f32[64,256]{1,0:T(8,128)S(1)}, f32[64,256]{1,0:T(8,128)S(1)}, u32[]{:S(2)}, u32[]{:S(2)}) collective-permute-start(f32[64,256]{1,0:T(8,128)S(1)} %shard_map.114.refs_0_), channel_id=1, source_target_pairs={{0,1},{1,0},{2,3},{3,2},{4,5},{5,4},{6,7},{7,6},{8,9},{9,8},{10,11... | collective-permute-start | bytes 196616 | tf_op jit(solution)/shard_map/ppermute | solution.py:33
  17.7 2.1 %collective-permute-start.7 = (f32[64,256]{1,0:T(8,128)S(1)}, f32[64,256]{1,0:T(8,128)S(1)}, u32[]{:S(2)}, u32[]{:S(2)}) collective-permute-start(f32[64,256]{1,0:T(8,128)S(1)} %shard_map.114.refs_0_), channel_id=1, source_target_pairs={{0,2},{1,3},{2,0},{3,1},{4,6},{5,7},{6,4},{7,5},{8,10},{9,11},{10,... | collective-permute-start | bytes 196616 | tf_op jit(solution)/shard_map/ppermute | solution.py:33
  19.8 1.4 %collective-permute-start.8 = (f32[64,256]{1,0:T(8,128)S(1)}, f32[64,256]{1,0:T(8,128)S(1)}, u32[]{:S(2)}, u32[]{:S(2)}) collective-permute-start(f32[64,256]{1,0:T(8,128)S(1)} %shard_map.114.refs_0_), channel_id=1, source_target_pairs={{0,3},{1,2},{2,1},{3,0},{4,7},{5,6},{6,5},{7,4},{8,11},{9,10},{10,... | collective-permute-start | bytes 196616 | tf_op jit(solution)/shard_map/ppermute | solution.py:33
  21.7 2.3 %collective-permute-start.9 = (f32[64,256]{1,0:T(8,128)S(1)}, f32[64,256]{1,0:T(8,128)S(1)}, u32[]{:S(2)}, u32[]{:S(2)}) collective-permute-start(f32[64,256]{1,0:T(8,128)S(1)} %shard_map.115.refs_1_), channel_id=1, source_target_pairs={{0,2},{1,3},{2,0},{3,1},{4,6},{5,7},{6,4},{7,5},{8,10},{9,11},{10,... | collective-permute-start | bytes 196616 | tf_op jit(solution)/shard_map/ppermute | solution.py:33
  24.0 0.7 collective-permute-start.13
  24.8 3.1 %collective-permute-done.7 = f32[64,256]{1,0:T(8,128)S(1)} collective-permute-done((f32[64,256]{1,0:T(8,128)S(1)}, f32[64,256]{1,0:T(8,128)S(1)}, u32[]{:S(2)}, u32[]{:S(2)}) %collective-permute-start.7) | collective-permute-done | bytes 65568 | tf_op jit(solution)/shard_map/ppermute | solution.py:33
  28.4 0.6 constant_dynamic-update-slice_fusion.51
  29.0 3.9 %collective-permute-start.11 = (f32[64,256]{1,0:T(8,128)S(1)}, f32[64,256]{1,0:T(8,128)S(1)}, u32[]{:S(2)}, u32[]{:S(2)}) collective-permute-start(f32[64,256]{1,0:T(8,128)S(1)} %get-tuple-element.53), channel_id=1, source_target_pairs={{0,2},{1,3},{2,0},{3,1},{4,6},{5,7},{6,4},{7,5},{8,10},{9,11},{10,... | collective-permute-start | bytes 196616 | tf_op jit(solution)/shard_map/ppermute | solution.py:33
  33.6 0.6 constant_dynamic-update-slice_fusion.43
  34.2 3.8 %collective-permute-start.16 = (f32[64,256]{1,0:T(8,128)S(1)}, f32[64,256]{1,0:T(8,128)S(1)}, u32[]{:S(2)}, u32[]{:S(2)}) collective-permute-start(f32[64,256]{1,0:T(8,128)S(1)} %get-tuple-element.56), channel_id=1, source_target_pairs={{0,2},{1,3},{2,0},{3,1},{4,6},{5,7},{6,4},{7,5},{8,10},{9,11},{10,... | collective-permute-start | bytes 196616 | tf_op jit(solution)/shard_map/ppermute | solution.py:33
  38.7 1.0 collective-permute-done.14
  40.4 2.8 %collective-permute-start.19 = (f32[64,256]{1,0:T(8,128)S(1)}, f32[64,256]{1,0:T(8,128)S(1)}, u32[]{:S(2)}, u32[]{:S(2)}) collective-permute-start(f32[64,256]{1,0:T(8,128)S(1)} %get-tuple-element.58.refs_2_), channel_id=1, source_target_pairs={{0,2},{1,3},{2,0},{3,1},{4,6},{5,7},{6,4},{7,5},{8,10},{9,11},{10,... | collective-permute-start | bytes 196616 | tf_op jit(solution)/shard_map/ppermute | solution.py:33
  43.2 0.7 collective-permute-start.20
  45.0 4.0 %collective-permute-start.21 = (f32[64,256]{1,0:T(8,128)S(1)}, f32[64,256]{1,0:T(8,128)S(1)}, u32[]{:S(2)}, u32[]{:S(2)}) collective-permute-start(f32[64,256]{1,0:T(8,128)S(1)} %get-tuple-element.62.refs_3_), channel_id=1, source_target_pairs={{0,2},{1,3},{2,0},{3,1},{4,6},{5,7},{6,4},{7,5},{8,10},{9,11},{10,... | collective-permute-start | bytes 196616 | tf_op jit(solution)/shard_map/ppermute | solution.py:33
  49.0 1.9 %collective-permute-start.25 = (f32[64,256]{1,0:T(8,128)S(1)}, f32[64,256]{1,0:T(8,128)S(1)}, u32[]{:S(2)}, u32[]{:S(2)}) collective-permute-start(f32[64,256]{1,0:T(8,128)S(1)} %get-tuple-element.62.refs_3_), channel_id=1, source_target_pairs={{0,3},{1,2},{2,1},{3,0},{4,7},{5,6},{6,5},{7,4},{8,11},{9,10},{10,... | collective-permute-start | bytes 196616 | tf_op jit(solution)/shard_map/ppermute | solution.py:33
  51.0 0.6 constant_dynamic-update-slice_fusion.35
  51.6 2.5 %collective-permute-start.23 = (f32[64,256]{1,0:T(8,128)S(1)}, f32[64,256]{1,0:T(8,128)S(1)}, u32[]{:S(2)}, u32[]{:S(2)}) collective-permute-start(f32[64,256]{1,0:T(8,128)S(1)} %get-tuple-element.61), channel_id=1, source_target_pairs={{0,2},{1,3},{2,0},{3,1},{4,6},{5,7},{6,4},{7,5},{8,10},{9,11},{10,... | collective-permute-start | bytes 196616 | tf_op jit(solution)/shard_map/ppermute | solution.py:33
  54.2 1.9 %collective-permute-start.26 = (f32[64,256]{1,0:T(8,128)S(1)}, f32[64,256]{1,0:T(8,128)S(1)}, u32[]{:S(2)}, u32[]{:S(2)}) collective-permute-start(f32[64,256]{1,0:T(8,128)S(1)} %get-tuple-element.61), channel_id=1, source_target_pairs={{0,3},{1,2},{2,1},{3,0},{4,7},{5,6},{6,5},{7,4},{8,11},{9,10},{10,... | collective-permute-start | bytes 196616 | tf_op jit(solution)/shard_map/ppermute | solution.py:33
  56.8 3.6 %collective-permute-start.28 = (f32[64,256]{1,0:T(8,128)S(1)}, f32[64,256]{1,0:T(8,128)S(1)}, u32[]{:S(2)}, u32[]{:S(2)}) collective-permute-start(f32[64,256]{1,0:T(8,128)S(1)} %get-tuple-element.64), channel_id=1, source_target_pairs={{0,2},{1,3},{2,0},{3,1},{4,6},{5,7},{6,4},{7,5},{8,10},{9,11},{10,... | collective-permute-start | bytes 196616 | tf_op jit(solution)/shard_map/ppermute | solution.py:33
  60.4 0.8 collective-permute-start.29
  62.0 3.6 %collective-permute-start.31 = (f32[64,256]{1,0:T(8,128)S(1)}, f32[64,256]{1,0:T(8,128)S(1)}, u32[]{:S(2)}, u32[]{:S(2)}) collective-permute-start(f32[64,256]{1,0:T(8,128)S(1)} %get-tuple-element.66.refs_4_), channel_id=1, source_target_pairs={{0,2},{1,3},{2,0},{3,1},{4,6},{5,7},{6,4},{7,5},{8,10},{9,11},{10,... | collective-permute-start | bytes 196616 | tf_op jit(solution)/shard_map/ppermute | solution.py:33
  65.6 0.8 collective-permute-start.32
  67.6 4.0 %collective-permute-start.33 = (f32[64,256]{1,0:T(8,128)S(1)}, f32[64,256]{1,0:T(8,128)S(1)}, u32[]{:S(2)}, u32[]{:S(2)}) collective-permute-start(f32[64,256]{1,0:T(8,128)S(1)} %get-tuple-element.70.refs_5_), channel_id=1, source_target_pairs={{0,2},{1,3},{2,0},{3,1},{4,6},{5,7},{6,4},{7,5},{8,10},{9,11},{10,... | collective-permute-start | bytes 196616 | tf_op jit(solution)/shard_map/ppermute | solution.py:33
  71.6 1.8 %collective-permute-start.37 = (f32[64,256]{1,0:T(8,128)S(1)}, f32[64,256]{1,0:T(8,128)S(1)}, u32[]{:S(2)}, u32[]{:S(2)}) collective-permute-start(f32[64,256]{1,0:T(8,128)S(1)} %get-tuple-element.70.refs_5_), channel_id=1, source_target_pairs={{0,3},{1,2},{2,1},{3,0},{4,7},{5,6},{6,5},{7,4},{8,11},{9,10},{10,... | collective-permute-start | bytes 196616 | tf_op jit(solution)/shard_map/ppermute | solution.py:33
  73.5 0.6 constant_dynamic-update-slice_fusion.19
  74.2 2.6 %collective-permute-start.35 = (f32[64,256]{1,0:T(8,128)S(1)}, f32[64,256]{1,0:T(8,128)S(1)}, u32[]{:S(2)}, u32[]{:S(2)}) collective-permute-start(f32[64,256]{1,0:T(8,128)S(1)} %get-tuple-element.69), channel_id=1, source_target_pairs={{0,2},{1,3},{2,0},{3,1},{4,6},{5,7},{6,4},{7,5},{8,10},{9,11},{10,... | collective-permute-start | bytes 196616 | tf_op jit(solution)/shard_map/ppermute | solution.py:33
  76.8 1.8 %collective-permute-start.38 = (f32[64,256]{1,0:T(8,128)S(1)}, f32[64,256]{1,0:T(8,128)S(1)}, u32[]{:S(2)}, u32[]{:S(2)}) collective-permute-start(f32[64,256]{1,0:T(8,128)S(1)} %get-tuple-element.69), channel_id=1, source_target_pairs={{0,3},{1,2},{2,1},{3,0},{4,7},{5,6},{6,5},{7,4},{8,11},{9,10},{10,... | collective-permute-start | bytes 196616 | tf_op jit(solution)/shard_map/ppermute | solution.py:33
  78.7 0.6 constant_dynamic-update-slice_fusion.11
  79.3 2.6 %collective-permute-start.40 = (f32[64,256]{1,0:T(8,128)S(1)}, f32[64,256]{1,0:T(8,128)S(1)}, u32[]{:S(2)}, u32[]{:S(2)}) collective-permute-start(f32[64,256]{1,0:T(8,128)S(1)} %get-tuple-element.72), channel_id=1, source_target_pairs={{0,2},{1,3},{2,0},{3,1},{4,6},{5,7},{6,4},{7,5},{8,10},{9,11},{10,... | collective-permute-start | bytes 196616 | tf_op jit(solution)/shard_map/ppermute | solution.py:33
  82.0 1.8 %collective-permute-start.41 = (f32[64,256]{1,0:T(8,128)S(1)}, f32[64,256]{1,0:T(8,128)S(1)}, u32[]{:S(2)}, u32[]{:S(2)}) collective-permute-start(f32[64,256]{1,0:T(8,128)S(1)} %get-tuple-element.72), channel_id=1, source_target_pairs={{0,3},{1,2},{2,1},{3,0},{4,7},{5,6},{6,5},{7,4},{8,11},{9,10},{10,... | collective-permute-start | bytes 196616 | tf_op jit(solution)/shard_map/ppermute | solution.py:33
  84.5 4.2 %collective-permute-start.43 = (f32[64,256]{1,0:T(8,128)S(1)}, f32[64,256]{1,0:T(8,128)S(1)}, u32[]{:S(2)}, u32[]{:S(2)}) collective-permute-start(f32[64,256]{1,0:T(8,128)S(1)} %get-tuple-element.74.refs_6_), channel_id=1, source_target_pairs={{0,2},{1,3},{2,0},{3,1},{4,6},{5,7},{6,4},{7,5},{8,10},{9,11},{10,... | collective-permute-start | bytes 196616 | tf_op jit(solution)/shard_map/ppermute | solution.py:33
  88.7 1.4 %collective-permute-start.44 = (f32[64,256]{1,0:T(8,128)S(1)}, f32[64,256]{1,0:T(8,128)S(1)}, u32[]{:S(2)}, u32[]{:S(2)}) collective-permute-start(f32[64,256]{1,0:T(8,128)S(1)} %get-tuple-element.74.refs_6_), channel_id=1, source_target_pairs={{0,3},{1,2},{2,1},{3,0},{4,7},{5,6},{6,5},{7,4},{8,11},{9,10},{10,... | collective-permute-start | bytes 196616 | tf_op jit(solution)/shard_map/ppermute | solution.py:33
  90.9 3.1 %collective-permute-start.46 = (f32[64,256]{1,0:T(8,128)S(1)}, f32[64,256]{1,0:T(8,128)S(1)}, u32[]{:S(2)}, u32[]{:S(2)}) collective-permute-start(f32[64,256]{1,0:T(8,128)S(1)} %get-tuple-element.76.refs_7_), channel_id=1, source_target_pairs={{0,2},{1,3},{2,0},{3,1},{4,6},{5,7},{6,4},{7,5},{8,10},{9,11},{10,... | collective-permute-start | bytes 196616 | tf_op jit(solution)/shard_map/ppermute | solution.py:33
  93.9 1.4 %collective-permute-start.47 = (f32[64,256]{1,0:T(8,128)S(1)}, f32[64,256]{1,0:T(8,128)S(1)}, u32[]{:S(2)}, u32[]{:S(2)}) collective-permute-start(f32[64,256]{1,0:T(8,128)S(1)} %get-tuple-element.76.refs_7_), channel_id=1, source_target_pairs={{0,3},{1,2},{2,1},{3,0},{4,7},{5,6},{6,5},{7,4},{8,11},{9,10},{10,... | collective-permute-start | bytes 196616 | tf_op jit(solution)/shard_map/ppermute | solution.py:33
  95.4 1.0 collective-permute-done.46
  96.4 1.2 shard_map.117.refs_0_
  97.6 2.7 %collective-permute-done.45 = f32[64,256]{1,0:T(8,128)S(1)} collective-permute-done((f32[64,256]{1,0:T(8,128)S(1)}, f32[64,256]{1,0:T(8,128)S(1)}, u32[]{:S(2)}, u32[]{:S(2)}) %collective-permute-start.45) | collective-permute-done | bytes 65568 | tf_op jit(solution)/shard_map/ppermute | solution.py:33
  100.3 1.2 shard_map.118
  101.6 1.3 collective-permute-done.48.refs_1_
  103.0 2.5 %collective-permute-start.49 = (f32[2,16,512]{2,1,0:T(8,128)S(1)}, f32[2,16,512]{2,1,0:T(8,128)S(1)}, u32[]{:S(2)}, u32[]{:S(2)}) collective-permute-start(f32[2,16,512]{2,1,0:T(8,128)S(1)} %get-tuple-element.82), channel_id=1, source_target_pairs={{0,24},{4,28},{8,16},{12,20},{16,8},{20,12},{24,0},{28,4},{1,25},{... | collective-permute-start | bytes 196616 | tf_op jit(solution)/shard_map/ppermute | solution.py:81
  106.5 1.0 shard_map.119
  107.5 0.7 collective-permute-done.49.refs_1_
  108.2 1.5 %collective-permute-done.50.refs_2_ = f32[2,16,512]{2,1,0:T(8,128)S(1)} collective-permute-done((f32[2,16,512]{2,1,0:T(8,128)S(1)}, f32[2,16,512]{2,1,0:T(8,128)S(1)}, u32[]{:S(2)}, u32[]{:S(2)}) %collective-permute-start.50) | collective-permute-done | bytes 65568 | tf_op jit(solution)/shard_map/ppermute | solution.py:81
  110.7 1.0 collective-permute-start.52
  111.7 1.4 %collective-permute-start.53 = (f32[16,1280]{1,0:T(8,128)S(1)}, f32[16,1280]{1,0:T(8,128)S(1)}, u32[]{:S(2)}, u32[]{:S(2)}) collective-permute-start(f32[16,1280]{1,0:T(8,128)S(1)} %get-tuple-element.88), channel_id=1, source_target_pairs={{0,3},{1,2},{2,1},{3,0},{4,7},{5,6},{6,5},{7,4},{8,11},{9,10},{10,... | collective-permute-start | bytes 245768 | tf_op jit(solution)/shard_map/ppermute | solution.py:33
  113.1 1.1 collective-permute-start.54
  114.7 3.7 %collective-permute-done.52.refs_1_ = f32[16,1280]{1,0:T(8,128)S(1)} collective-permute-done((f32[16,1280]{1,0:T(8,128)S(1)}, f32[16,1280]{1,0:T(8,128)S(1)}, u32[]{:S(2)}, u32[]{:S(2)}) %collective-permute-start.52) | collective-permute-done | bytes 81952 | tf_op jit(solution)/shard_map/ppermute | solution.py:33
  118.4 0.7 collective-permute-done.54.refs_3_
  119.5 1.6 %collective-permute-start.55 = (f32[16,256]{1,0:T(8,128)S(1)}, f32[16,256]{1,0:T(8,128)S(1)}, u32[]{:S(2)}, u32[]{:S(2)}) collective-permute-start(f32[16,256]{1,0:T(8,128)S(1)} %get-tuple-element.92.refs_0_.refs_6_), channel_id=1, source_target_pairs={{0,2},{1,3},{2,0},{3,1},{4,6},{5,7},{6,4},{7,5},{8,10},{9,11},{10,... | collective-permute-start | bytes 49160 | tf_op jit(solution)/shard_map/ppermute | solution.py:33
  121.1 1.5 %collective-permute-start.56 = (f32[16,256]{1,0:T(8,128)S(1)}, f32[16,256]{1,0:T(8,128)S(1)}, u32[]{:S(2)}, u32[]{:S(2)}) collective-permute-start(f32[16,256]{1,0:T(8,128)S(1)} %get-tuple-element.92.refs_0_.refs_6_), channel_id=1, source_target_pairs={{0,3},{1,2},{2,1},{3,0},{4,7},{5,6},{6,5},{7,4},{8,11},{9,10},{10,... | collective-permute-start | bytes 49160 | tf_op jit(solution)/shard_map/ppermute | solution.py:33
  123.0 1.2 collective-permute-done.55.refs_1_
  124.2 2.5 %collective-permute-done.56.refs_2_ = f32[16,256]{1,0:T(8,128)S(1)} collective-permute-done((f32[16,256]{1,0:T(8,128)S(1)}, f32[16,256]{1,0:T(8,128)S(1)}, u32[]{:S(2)}, u32[]{:S(2)}) %collective-permute-start.56) | collective-permute-done | bytes 16416 | tf_op jit(solution)/shard_map/ppermute | solution.py:33
  127.0 0.8 collective-permute-start.58
  127.8 1.7 %collective-permute-start.59 = (f32[16,256]{1,0:T(8,128)S(1)}, f32[16,256]{1,0:T(8,128)S(1)}, u32[]{:S(2)}, u32[]{:S(2)}) collective-permute-start(f32[16,256]{1,0:T(8,128)S(1)} %shard_map.124.refs_0_), channel_id=1, source_target_pairs={{0,3},{1,2},{2,1},{3,0},{4,7},{5,6},{6,5},{7,4},{8,11},{9,10},{10,... | collective-permute-start | bytes 49160 | tf_op jit(solution)/shard_map/ppermute | solution.py:33
  129.5 1.0 collective-permute-start.60
  130.5 1.1 collective-permute-done.58.refs_1_
  131.7 1.7 %collective-permute-done.59.refs_2_ = f32[16,256]{1,0:T(8,128)S(1)} collective-permute-done((f32[16,256]{1,0:T(8,128)S(1)}, f32[16,256]{1,0:T(8,128)S(1)}, u32[]{:S(2)}, u32[]{:S(2)}) %collective-permute-start.59) | collective-permute-done | bytes 16416 | tf_op jit(solution)/shard_map/ppermute | solution.py:33
  133.4 1.0 shard_map.125
  (162 shorter events, 12.8 us)
Async XLA Ops:
  1.7 26.2 %copy-start.3 = (f32[1,4,256,128]{3,2,1,0:T(8,128)S(1)}, f32[1,4,256,128]{3,2,1,0:T(8,128)}, u32[]{:S(2)}) copy-start(f32[1,4,256,128]{3,2,1,0:T(8,128)} %rhs_ref.3) | copy-start | bytes 1572868
  1.9 10.1 %collective-permute-start = (f32[64,256]{1,0:T(8,128)S(1)}, f32[64,256]{1,0:T(8,128)S(1)}, u32[]{:S(2)}, u32[]{:S(2)}) collective-permute-start(f32[64,256]{1,0:T(8,128)S(1)} %get-tuple-element.49.refs_0_), channel_id=1, source_target_pairs={{0,1},{1,0},{2,3},{3,2},{4,5},{5,4},{6,7},{7,6},{8,9},{9,8},{10,11... | collective-permute-start | bytes 196616 | tf_op jit(solution)/shard_map/ppermute | solution.py:33
  5.0 9.1 %collective-permute-start.1 = (f32[64,256]{1,0:T(8,128)S(1)}, f32[64,256]{1,0:T(8,128)S(1)}, u32[]{:S(2)}, u32[]{:S(2)}) collective-permute-start(f32[64,256]{1,0:T(8,128)S(1)} %get-tuple-element.49.refs_0_), channel_id=1, source_target_pairs={{0,2},{1,3},{2,0},{3,1},{4,6},{5,7},{6,4},{7,5},{8,10},{9,11},{10,... | collective-permute-start | bytes 196616 | tf_op jit(solution)/shard_map/ppermute | solution.py:33
  7.6 6.6 %collective-permute-start.2 = (f32[64,256]{1,0:T(8,128)S(1)}, f32[64,256]{1,0:T(8,128)S(1)}, u32[]{:S(2)}, u32[]{:S(2)}) collective-permute-start(f32[64,256]{1,0:T(8,128)S(1)} %get-tuple-element.49.refs_0_), channel_id=1, source_target_pairs={{0,3},{1,2},{2,1},{3,0},{4,7},{5,6},{6,5},{7,4},{8,11},{9,10},{10,... | collective-permute-start | bytes 196616 | tf_op jit(solution)/shard_map/ppermute | solution.py:33
  7.6 12.2 %collective-permute-start.3 = (f32[64,256]{1,0:T(8,128)S(1)}, f32[64,256]{1,0:T(8,128)S(1)}, u32[]{:S(2)}, u32[]{:S(2)}) collective-permute-start(f32[64,256]{1,0:T(8,128)S(1)} %get-tuple-element.50.refs_0_), channel_id=1, source_target_pairs={{0,1},{1,0},{2,3},{3,2},{4,5},{5,4},{6,7},{7,6},{8,9},{9,8},{10,11... | collective-permute-start | bytes 196616 | tf_op jit(solution)/shard_map/ppermute | solution.py:33
  8.5 12.7 %collective-permute-start.4 = (f32[64,256]{1,0:T(8,128)S(1)}, f32[64,256]{1,0:T(8,128)S(1)}, u32[]{:S(2)}, u32[]{:S(2)}) collective-permute-start(f32[64,256]{1,0:T(8,128)S(1)} %get-tuple-element.50.refs_0_), channel_id=1, source_target_pairs={{0,2},{1,3},{2,0},{3,1},{4,6},{5,7},{6,4},{7,5},{8,10},{9,11},{10,... | collective-permute-start | bytes 196616 | tf_op jit(solution)/shard_map/ppermute | solution.py:33
  12.0 9.2 %collective-permute-start.5 = (f32[64,256]{1,0:T(8,128)S(1)}, f32[64,256]{1,0:T(8,128)S(1)}, u32[]{:S(2)}, u32[]{:S(2)}) collective-permute-start(f32[64,256]{1,0:T(8,128)S(1)} %get-tuple-element.50.refs_0_), channel_id=1, source_target_pairs={{0,3},{1,2},{2,1},{3,0},{4,7},{5,6},{6,5},{7,4},{8,11},{9,10},{10,... | collective-permute-start | bytes 196616 | tf_op jit(solution)/shard_map/ppermute | solution.py:33
  14.6 13.2 %collective-permute-start.6 = (f32[64,256]{1,0:T(8,128)S(1)}, f32[64,256]{1,0:T(8,128)S(1)}, u32[]{:S(2)}, u32[]{:S(2)}) collective-permute-start(f32[64,256]{1,0:T(8,128)S(1)} %shard_map.114.refs_0_), channel_id=1, source_target_pairs={{0,1},{1,0},{2,3},{3,2},{4,5},{5,4},{6,7},{7,6},{8,9},{9,8},{10,11... | collective-permute-start | bytes 196616 | tf_op jit(solution)/shard_map/ppermute | solution.py:33
  17.7 10.2 %collective-permute-start.7 = (f32[64,256]{1,0:T(8,128)S(1)}, f32[64,256]{1,0:T(8,128)S(1)}, u32[]{:S(2)}, u32[]{:S(2)}) collective-permute-start(f32[64,256]{1,0:T(8,128)S(1)} %shard_map.114.refs_0_), channel_id=1, source_target_pairs={{0,2},{1,3},{2,0},{3,1},{4,6},{5,7},{6,4},{7,5},{8,10},{9,11},{10,... | collective-permute-start | bytes 196616 | tf_op jit(solution)/shard_map/ppermute | solution.py:33
  19.8 8.5 %collective-permute-start.8 = (f32[64,256]{1,0:T(8,128)S(1)}, f32[64,256]{1,0:T(8,128)S(1)}, u32[]{:S(2)}, u32[]{:S(2)}) collective-permute-start(f32[64,256]{1,0:T(8,128)S(1)} %shard_map.114.refs_0_), channel_id=1, source_target_pairs={{0,3},{1,2},{2,1},{3,0},{4,7},{5,6},{6,5},{7,4},{8,11},{9,10},{10,... | collective-permute-start | bytes 196616 | tf_op jit(solution)/shard_map/ppermute | solution.py:33
  21.7 11.8 %collective-permute-start.9 = (f32[64,256]{1,0:T(8,128)S(1)}, f32[64,256]{1,0:T(8,128)S(1)}, u32[]{:S(2)}, u32[]{:S(2)}) collective-permute-start(f32[64,256]{1,0:T(8,128)S(1)} %shard_map.115.refs_1_), channel_id=1, source_target_pairs={{0,2},{1,3},{2,0},{3,1},{4,6},{5,7},{6,4},{7,5},{8,10},{9,11},{10,... | collective-permute-start | bytes 196616 | tf_op jit(solution)/shard_map/ppermute | solution.py:33
  24.0 9.6 %collective-permute-start.13 = (f32[64,256]{1,0:T(8,128)S(1)}, f32[64,256]{1,0:T(8,128)S(1)}, u32[]{:S(2)}, u32[]{:S(2)}) collective-permute-start(f32[64,256]{1,0:T(8,128)S(1)} %shard_map.115.refs_1_), channel_id=1, source_target_pairs={{0,3},{1,2},{2,1},{3,0},{4,7},{5,6},{6,5},{7,4},{8,11},{9,10},{10,... | collective-permute-start | bytes 196616 | tf_op jit(solution)/shard_map/ppermute | solution.py:33
  27.9 5.6 %collective-permute-start.12 = (f32[64,256]{1,0:T(8,128)S(1)}, f32[64,256]{1,0:T(8,128)S(1)}, u32[]{:S(2)}, u32[]{:S(2)}) collective-permute-start(f32[64,256]{1,0:T(8,128)S(1)} %shard_map.115.refs_1_), channel_id=1, source_target_pairs={{0,1},{1,0},{2,3},{3,2},{4,5},{5,4},{6,7},{7,6},{8,9},{9,8},{10,11... | collective-permute-start | bytes 196616 | tf_op jit(solution)/shard_map/ppermute | solution.py:33
  29.0 9.6 %collective-permute-start.11 = (f32[64,256]{1,0:T(8,128)S(1)}, f32[64,256]{1,0:T(8,128)S(1)}, u32[]{:S(2)}, u32[]{:S(2)}) collective-permute-start(f32[64,256]{1,0:T(8,128)S(1)} %get-tuple-element.53), channel_id=1, source_target_pairs={{0,2},{1,3},{2,0},{3,1},{4,6},{5,7},{6,4},{7,5},{8,10},{9,11},{10,... | collective-permute-start | bytes 196616 | tf_op jit(solution)/shard_map/ppermute | solution.py:33
  32.9 6.8 %collective-permute-start.14 = (f32[64,256]{1,0:T(8,128)S(1)}, f32[64,256]{1,0:T(8,128)S(1)}, u32[]{:S(2)}, u32[]{:S(2)}) collective-permute-start(f32[64,256]{1,0:T(8,128)S(1)} %get-tuple-element.53), channel_id=1, source_target_pairs={{0,3},{1,2},{2,1},{3,0},{4,7},{5,6},{6,5},{7,4},{8,11},{9,10},{10,... | collective-permute-start | bytes 196616 | tf_op jit(solution)/shard_map/ppermute | solution.py:33
  33.4 5.2 %collective-permute-start.10 = (f32[64,256]{1,0:T(8,128)S(1)}, f32[64,256]{1,0:T(8,128)S(1)}, u32[]{:S(2)}, u32[]{:S(2)}) collective-permute-start(f32[64,256]{1,0:T(8,128)S(1)} %get-tuple-element.53), channel_id=1, source_target_pairs={{0,1},{1,0},{2,3},{3,2},{4,5},{5,4},{6,7},{7,6},{8,9},{9,8},{10,11... | collective-permute-start | bytes 196616 | tf_op jit(solution)/shard_map/ppermute | solution.py:33
  34.2 9.7 %collective-permute-start.16 = (f32[64,256]{1,0:T(8,128)S(1)}, f32[64,256]{1,0:T(8,128)S(1)}, u32[]{:S(2)}, u32[]{:S(2)}) collective-permute-start(f32[64,256]{1,0:T(8,128)S(1)} %get-tuple-element.56), channel_id=1, source_target_pairs={{0,2},{1,3},{2,0},{3,1},{4,6},{5,7},{6,4},{7,5},{8,10},{9,11},{10,... | collective-permute-start | bytes 196616 | tf_op jit(solution)/shard_map/ppermute | solution.py:33
  38.0 6.3 %collective-permute-start.17 = (f32[64,256]{1,0:T(8,128)S(1)}, f32[64,256]{1,0:T(8,128)S(1)}, u32[]{:S(2)}, u32[]{:S(2)}) collective-permute-start(f32[64,256]{1,0:T(8,128)S(1)} %get-tuple-element.56), channel_id=1, source_target_pairs={{0,3},{1,2},{2,1},{3,0},{4,7},{5,6},{6,5},{7,4},{8,11},{9,10},{10,... | collective-permute-start | bytes 196616 | tf_op jit(solution)/shard_map/ppermute | solution.py:33
  38.6 5.7 %collective-permute-start.15 = (f32[64,256]{1,0:T(8,128)S(1)}, f32[64,256]{1,0:T(8,128)S(1)}, u32[]{:S(2)}, u32[]{:S(2)}) collective-permute-start(f32[64,256]{1,0:T(8,128)S(1)} %get-tuple-element.56), channel_id=1, source_target_pairs={{0,1},{1,0},{2,3},{3,2},{4,5},{5,4},{6,7},{7,6},{8,9},{9,8},{10,11... | collective-permute-start | bytes 196616 | tf_op jit(solution)/shard_map/ppermute | solution.py:33
  40.4 10.5 %collective-permute-start.19 = (f32[64,256]{1,0:T(8,128)S(1)}, f32[64,256]{1,0:T(8,128)S(1)}, u32[]{:S(2)}, u32[]{:S(2)}) collective-permute-start(f32[64,256]{1,0:T(8,128)S(1)} %get-tuple-element.58.refs_2_), channel_id=1, source_target_pairs={{0,2},{1,3},{2,0},{3,1},{4,6},{5,7},{6,4},{7,5},{8,10},{9,11},{10,... | collective-permute-start | bytes 196616 | tf_op jit(solution)/shard_map/ppermute | solution.py:33
  43.2 7.7 %collective-permute-start.20 = (f32[64,256]{1,0:T(8,128)S(1)}, f32[64,256]{1,0:T(8,128)S(1)}, u32[]{:S(2)}, u32[]{:S(2)}) collective-permute-start(f32[64,256]{1,0:T(8,128)S(1)} %get-tuple-element.58.refs_2_), channel_id=1, source_target_pairs={{0,3},{1,2},{2,1},{3,0},{4,7},{5,6},{6,5},{7,4},{8,11},{9,10},{10,... | collective-permute-start | bytes 196616 | tf_op jit(solution)/shard_map/ppermute | solution.py:33
  43.9 7.0 %collective-permute-start.18 = (f32[64,256]{1,0:T(8,128)S(1)}, f32[64,256]{1,0:T(8,128)S(1)}, u32[]{:S(2)}, u32[]{:S(2)}) collective-permute-start(f32[64,256]{1,0:T(8,128)S(1)} %get-tuple-element.58.refs_2_), channel_id=1, source_target_pairs={{0,1},{1,0},{2,3},{3,2},{4,5},{5,4},{6,7},{7,6},{8,9},{9,8},{10,11... | collective-permute-start | bytes 196616 | tf_op jit(solution)/shard_map/ppermute | solution.py:33
  45.0 11.0 %collective-permute-start.21 = (f32[64,256]{1,0:T(8,128)S(1)}, f32[64,256]{1,0:T(8,128)S(1)}, u32[]{:S(2)}, u32[]{:S(2)}) collective-permute-start(f32[64,256]{1,0:T(8,128)S(1)} %get-tuple-element.62.refs_3_), channel_id=1, source_target_pairs={{0,2},{1,3},{2,0},{3,1},{4,6},{5,7},{6,4},{7,5},{8,10},{9,11},{10,... | collective-permute-start | bytes 196616 | tf_op jit(solution)/shard_map/ppermute | solution.py:33
  49.0 7.1 %collective-permute-start.25 = (f32[64,256]{1,0:T(8,128)S(1)}, f32[64,256]{1,0:T(8,128)S(1)}, u32[]{:S(2)}, u32[]{:S(2)}) collective-permute-start(f32[64,256]{1,0:T(8,128)S(1)} %get-tuple-element.62.refs_3_), channel_id=1, source_target_pairs={{0,3},{1,2},{2,1},{3,0},{4,7},{5,6},{6,5},{7,4},{8,11},{9,10},{10,... | collective-permute-start | bytes 196616 | tf_op jit(solution)/shard_map/ppermute | solution.py:33
  50.9 5.2 %collective-permute-start.24 = (f32[64,256]{1,0:T(8,128)S(1)}, f32[64,256]{1,0:T(8,128)S(1)}, u32[]{:S(2)}, u32[]{:S(2)}) collective-permute-start(f32[64,256]{1,0:T(8,128)S(1)} %get-tuple-element.62.refs_3_), channel_id=1, source_target_pairs={{0,1},{1,0},{2,3},{3,2},{4,5},{5,4},{6,7},{7,6},{8,9},{9,8},{10,11... | collective-permute-start | bytes 196616 | tf_op jit(solution)/shard_map/ppermute | solution.py:33
  51.6 9.6 %collective-permute-start.23 = (f32[64,256]{1,0:T(8,128)S(1)}, f32[64,256]{1,0:T(8,128)S(1)}, u32[]{:S(2)}, u32[]{:S(2)}) collective-permute-start(f32[64,256]{1,0:T(8,128)S(1)} %get-tuple-element.61), channel_id=1, source_target_pairs={{0,2},{1,3},{2,0},{3,1},{4,6},{5,7},{6,4},{7,5},{8,10},{9,11},{10,... | collective-permute-start | bytes 196616 | tf_op jit(solution)/shard_map/ppermute | solution.py:33
  54.2 7.1 %collective-permute-start.26 = (f32[64,256]{1,0:T(8,128)S(1)}, f32[64,256]{1,0:T(8,128)S(1)}, u32[]{:S(2)}, u32[]{:S(2)}) collective-permute-start(f32[64,256]{1,0:T(8,128)S(1)} %get-tuple-element.61), channel_id=1, source_target_pairs={{0,3},{1,2},{2,1},{3,0},{4,7},{5,6},{6,5},{7,4},{8,11},{9,10},{10,... | collective-permute-start | bytes 196616 | tf_op jit(solution)/shard_map/ppermute | solution.py:33
  56.1 5.2 %collective-permute-start.22 = (f32[64,256]{1,0:T(8,128)S(1)}, f32[64,256]{1,0:T(8,128)S(1)}, u32[]{:S(2)}, u32[]{:S(2)}) collective-permute-start(f32[64,256]{1,0:T(8,128)S(1)} %get-tuple-element.61), channel_id=1, source_target_pairs={{0,1},{1,0},{2,3},{3,2},{4,5},{5,4},{6,7},{7,6},{8,9},{9,8},{10,11... | collective-permute-start | bytes 196616 | tf_op jit(solution)/shard_map/ppermute | solution.py:33
  56.8 9.6 %collective-permute-start.28 = (f32[64,256]{1,0:T(8,128)S(1)}, f32[64,256]{1,0:T(8,128)S(1)}, u32[]{:S(2)}, u32[]{:S(2)}) collective-permute-start(f32[64,256]{1,0:T(8,128)S(1)} %get-tuple-element.64), channel_id=1, source_target_pairs={{0,2},{1,3},{2,0},{3,1},{4,6},{5,7},{6,4},{7,5},{8,10},{9,11},{10,... | collective-permute-start | bytes 196616 | tf_op jit(solution)/shard_map/ppermute | solution.py:33
  60.4 6.5 %collective-permute-start.29 = (f32[64,256]{1,0:T(8,128)S(1)}, f32[64,256]{1,0:T(8,128)S(1)}, u32[]{:S(2)}, u32[]{:S(2)}) collective-permute-start(f32[64,256]{1,0:T(8,128)S(1)} %get-tuple-element.64), channel_id=1, source_target_pairs={{0,3},{1,2},{2,1},{3,0},{4,7},{5,6},{6,5},{7,4},{8,11},{9,10},{10,... | collective-permute-start | bytes 196616 | tf_op jit(solution)/shard_map/ppermute | solution.py:33
  61.3 5.7 %collective-permute-start.27 = (f32[64,256]{1,0:T(8,128)S(1)}, f32[64,256]{1,0:T(8,128)S(1)}, u32[]{:S(2)}, u32[]{:S(2)}) collective-permute-start(f32[64,256]{1,0:T(8,128)S(1)} %get-tuple-element.64), channel_id=1, source_target_pairs={{0,1},{1,0},{2,3},{3,2},{4,5},{5,4},{6,7},{7,6},{8,9},{9,8},{10,11... | collective-permute-start | bytes 196616 | tf_op jit(solution)/shard_map/ppermute | solution.py:33
  62.0 11.4 %collective-permute-start.31 = (f32[64,256]{1,0:T(8,128)S(1)}, f32[64,256]{1,0:T(8,128)S(1)}, u32[]{:S(2)}, u32[]{:S(2)}) collective-permute-start(f32[64,256]{1,0:T(8,128)S(1)} %get-tuple-element.66.refs_4_), channel_id=1, source_target_pairs={{0,2},{1,3},{2,0},{3,1},{4,6},{5,7},{6,4},{7,5},{8,10},{9,11},{10,... | collective-permute-start | bytes 196616 | tf_op jit(solution)/shard_map/ppermute | solution.py:33
  65.6 7.9 %collective-permute-start.32 = (f32[64,256]{1,0:T(8,128)S(1)}, f32[64,256]{1,0:T(8,128)S(1)}, u32[]{:S(2)}, u32[]{:S(2)}) collective-permute-start(f32[64,256]{1,0:T(8,128)S(1)} %get-tuple-element.66.refs_4_), channel_id=1, source_target_pairs={{0,3},{1,2},{2,1},{3,0},{4,7},{5,6},{6,5},{7,4},{8,11},{9,10},{10,... | collective-permute-start | bytes 196616 | tf_op jit(solution)/shard_map/ppermute | solution.py:33
  66.4 7.0 %collective-permute-start.30 = (f32[64,256]{1,0:T(8,128)S(1)}, f32[64,256]{1,0:T(8,128)S(1)}, u32[]{:S(2)}, u32[]{:S(2)}) collective-permute-start(f32[64,256]{1,0:T(8,128)S(1)} %get-tuple-element.66.refs_4_), channel_id=1, source_target_pairs={{0,1},{1,0},{2,3},{3,2},{4,5},{5,4},{6,7},{7,6},{8,9},{9,8},{10,11... | collective-permute-start | bytes 196616 | tf_op jit(solution)/shard_map/ppermute | solution.py:33
  67.6 11.0 %collective-permute-start.33 = (f32[64,256]{1,0:T(8,128)S(1)}, f32[64,256]{1,0:T(8,128)S(1)}, u32[]{:S(2)}, u32[]{:S(2)}) collective-permute-start(f32[64,256]{1,0:T(8,128)S(1)} %get-tuple-element.70.refs_5_), channel_id=1, source_target_pairs={{0,2},{1,3},{2,0},{3,1},{4,6},{5,7},{6,4},{7,5},{8,10},{9,11},{10,... | collective-permute-start | bytes 196616 | tf_op jit(solution)/shard_map/ppermute | solution.py:33
  71.6 7.1 %collective-permute-start.37 = (f32[64,256]{1,0:T(8,128)S(1)}, f32[64,256]{1,0:T(8,128)S(1)}, u32[]{:S(2)}, u32[]{:S(2)}) collective-permute-start(f32[64,256]{1,0:T(8,128)S(1)} %get-tuple-element.70.refs_5_), channel_id=1, source_target_pairs={{0,3},{1,2},{2,1},{3,0},{4,7},{5,6},{6,5},{7,4},{8,11},{9,10},{10,... | collective-permute-start | bytes 196616 | tf_op jit(solution)/shard_map/ppermute | solution.py:33
  73.4 5.2 %collective-permute-start.36 = (f32[64,256]{1,0:T(8,128)S(1)}, f32[64,256]{1,0:T(8,128)S(1)}, u32[]{:S(2)}, u32[]{:S(2)}) collective-permute-start(f32[64,256]{1,0:T(8,128)S(1)} %get-tuple-element.70.refs_5_), channel_id=1, source_target_pairs={{0,1},{1,0},{2,3},{3,2},{4,5},{5,4},{6,7},{7,6},{8,9},{9,8},{10,11... | collective-permute-start | bytes 196616 | tf_op jit(solution)/shard_map/ppermute | solution.py:33
  74.2 9.6 %collective-permute-start.35 = (f32[64,256]{1,0:T(8,128)S(1)}, f32[64,256]{1,0:T(8,128)S(1)}, u32[]{:S(2)}, u32[]{:S(2)}) collective-permute-start(f32[64,256]{1,0:T(8,128)S(1)} %get-tuple-element.69), channel_id=1, source_target_pairs={{0,2},{1,3},{2,0},{3,1},{4,6},{5,7},{6,4},{7,5},{8,10},{9,11},{10,... | collective-permute-start | bytes 196616 | tf_op jit(solution)/shard_map/ppermute | solution.py:33
  76.8 7.1 %collective-permute-start.38 = (f32[64,256]{1,0:T(8,128)S(1)}, f32[64,256]{1,0:T(8,128)S(1)}, u32[]{:S(2)}, u32[]{:S(2)}) collective-permute-start(f32[64,256]{1,0:T(8,128)S(1)} %get-tuple-element.69), channel_id=1, source_target_pairs={{0,3},{1,2},{2,1},{3,0},{4,7},{5,6},{6,5},{7,4},{8,11},{9,10},{10,... | collective-permute-start | bytes 196616 | tf_op jit(solution)/shard_map/ppermute | solution.py:33
  78.6 5.2 %collective-permute-start.34 = (f32[64,256]{1,0:T(8,128)S(1)}, f32[64,256]{1,0:T(8,128)S(1)}, u32[]{:S(2)}, u32[]{:S(2)}) collective-permute-start(f32[64,256]{1,0:T(8,128)S(1)} %get-tuple-element.69), channel_id=1, source_target_pairs={{0,1},{1,0},{2,3},{3,2},{4,5},{5,4},{6,7},{7,6},{8,9},{9,8},{10,11... | collective-permute-start | bytes 196616 | tf_op jit(solution)/shard_map/ppermute | solution.py:33
  79.3 10.8 %collective-permute-start.40 = (f32[64,256]{1,0:T(8,128)S(1)}, f32[64,256]{1,0:T(8,128)S(1)}, u32[]{:S(2)}, u32[]{:S(2)}) collective-permute-start(f32[64,256]{1,0:T(8,128)S(1)} %get-tuple-element.72), channel_id=1, source_target_pairs={{0,2},{1,3},{2,0},{3,1},{4,6},{5,7},{6,4},{7,5},{8,10},{9,11},{10,... | collective-permute-start | bytes 196616 | tf_op jit(solution)/shard_map/ppermute | solution.py:33
  82.0 8.2 %collective-permute-start.41 = (f32[64,256]{1,0:T(8,128)S(1)}, f32[64,256]{1,0:T(8,128)S(1)}, u32[]{:S(2)}, u32[]{:S(2)}) collective-permute-start(f32[64,256]{1,0:T(8,128)S(1)} %get-tuple-element.72), channel_id=1, source_target_pairs={{0,3},{1,2},{2,1},{3,0},{4,7},{5,6},{6,5},{7,4},{8,11},{9,10},{10,... | collective-permute-start | bytes 196616 | tf_op jit(solution)/shard_map/ppermute | solution.py:33
  83.8 6.3 %collective-permute-start.39 = (f32[64,256]{1,0:T(8,128)S(1)}, f32[64,256]{1,0:T(8,128)S(1)}, u32[]{:S(2)}, u32[]{:S(2)}) collective-permute-start(f32[64,256]{1,0:T(8,128)S(1)} %get-tuple-element.72), channel_id=1, source_target_pairs={{0,1},{1,0},{2,3},{3,2},{4,5},{5,4},{6,7},{7,6},{8,9},{9,8},{10,11... | collective-permute-start | bytes 196616 | tf_op jit(solution)/shard_map/ppermute | solution.py:33
  84.5 10.8 %collective-permute-start.43 = (f32[64,256]{1,0:T(8,128)S(1)}, f32[64,256]{1,0:T(8,128)S(1)}, u32[]{:S(2)}, u32[]{:S(2)}) collective-permute-start(f32[64,256]{1,0:T(8,128)S(1)} %get-tuple-element.74.refs_6_), channel_id=1, source_target_pairs={{0,2},{1,3},{2,0},{3,1},{4,6},{5,7},{6,4},{7,5},{8,10},{9,11},{10,... | collective-permute-start | bytes 196616 | tf_op jit(solution)/shard_map/ppermute | solution.py:33
  88.7 6.6 %collective-permute-start.44 = (f32[64,256]{1,0:T(8,128)S(1)}, f32[64,256]{1,0:T(8,128)S(1)}, u32[]{:S(2)}, u32[]{:S(2)}) collective-permute-start(f32[64,256]{1,0:T(8,128)S(1)} %get-tuple-element.74.refs_6_), channel_id=1, source_target_pairs={{0,3},{1,2},{2,1},{3,0},{4,7},{5,6},{6,5},{7,4},{8,11},{9,10},{10,... | collective-permute-start | bytes 196616 | tf_op jit(solution)/shard_map/ppermute | solution.py:33
  90.1 5.2 %collective-permute-start.42 = (f32[64,256]{1,0:T(8,128)S(1)}, f32[64,256]{1,0:T(8,128)S(1)}, u32[]{:S(2)}, u32[]{:S(2)}) collective-permute-start(f32[64,256]{1,0:T(8,128)S(1)} %get-tuple-element.74.refs_6_), channel_id=1, source_target_pairs={{0,1},{1,0},{2,3},{3,2},{4,5},{5,4},{6,7},{7,6},{8,9},{9,8},{10,11... | collective-permute-start | bytes 196616 | tf_op jit(solution)/shard_map/ppermute | solution.py:33
  90.9 5.5 %collective-permute-start.46 = (f32[64,256]{1,0:T(8,128)S(1)}, f32[64,256]{1,0:T(8,128)S(1)}, u32[]{:S(2)}, u32[]{:S(2)}) collective-permute-start(f32[64,256]{1,0:T(8,128)S(1)} %get-tuple-element.76.refs_7_), channel_id=1, source_target_pairs={{0,2},{1,3},{2,0},{3,1},{4,6},{5,7},{6,4},{7,5},{8,10},{9,11},{10,... | collective-permute-start | bytes 196616 | tf_op jit(solution)/shard_map/ppermute | solution.py:33
  93.9 6.4 %collective-permute-start.47 = (f32[64,256]{1,0:T(8,128)S(1)}, f32[64,256]{1,0:T(8,128)S(1)}, u32[]{:S(2)}, u32[]{:S(2)}) collective-permute-start(f32[64,256]{1,0:T(8,128)S(1)} %get-tuple-element.76.refs_7_), channel_id=1, source_target_pairs={{0,3},{1,2},{2,1},{3,0},{4,7},{5,6},{6,5},{7,4},{8,11},{9,10},{10,... | collective-permute-start | bytes 196616 | tf_op jit(solution)/shard_map/ppermute | solution.py:33
  95.3 5.0 %collective-permute-start.45 = (f32[64,256]{1,0:T(8,128)S(1)}, f32[64,256]{1,0:T(8,128)S(1)}, u32[]{:S(2)}, u32[]{:S(2)}) collective-permute-start(f32[64,256]{1,0:T(8,128)S(1)} %get-tuple-element.76.refs_7_), channel_id=1, source_target_pairs={{0,1},{1,0},{2,3},{3,2},{4,5},{5,4},{6,7},{7,6},{8,9},{9,8},{10,11... | collective-permute-start | bytes 196616 | tf_op jit(solution)/shard_map/ppermute | solution.py:33
  96.3 17.9 %copy-start.1 = (f32[2,256,1024]{2,1,0:T(8,128)S(1)}, f32[2,256,1024]{2,1,0:T(8,128)}, u32[]{:S(2)}) copy-start(f32[2,256,1024]{2,1,0:T(8,128)} %refs_0_.1) | copy-start | bytes 6291460
  96.4 17.9 %copy-start.4 = (f32[1,256,1024]{2,1,0:T(8,128)S(1)}, f32[1,256,1024]{2,1,0:T(8,128)}, u32[]{:S(2)}) copy-start(f32[1,256,1024]{2,1,0:T(8,128)} %refs_1_.1) | copy-start | bytes 3145732
  101.5 1.4 %collective-permute-start.48 = (f32[4,16,512]{2,1,0:T(8,128)S(1)}, f32[4,16,512]{2,1,0:T(8,128)S(1)}, u32[]{:S(2)}, u32[]{:S(2)}) collective-permute-start(f32[4,16,512]{2,1,0:T(8,128)S(1)} %get-tuple-element.80), channel_id=1, source_target_pairs={{0,4},{4,0},{8,12},{12,8},{16,20},{20,16},{24,28},{28,24},{1,5},{5... | collective-permute-start | bytes 393224 | tf_op jit(solution)/shard_map/ppermute | solution.py:281
  103.0 5.3 %collective-permute-start.49 = (f32[2,16,512]{2,1,0:T(8,128)S(1)}, f32[2,16,512]{2,1,0:T(8,128)S(1)}, u32[]{:S(2)}, u32[]{:S(2)}) collective-permute-start(f32[2,16,512]{2,1,0:T(8,128)S(1)} %get-tuple-element.82), channel_id=1, source_target_pairs={{0,24},{4,28},{8,16},{12,20},{16,8},{20,12},{24,0},{28,4},{1,25},{... | collective-permute-start | bytes 196616 | tf_op jit(solution)/shard_map/ppermute | solution.py:81
  105.5 4.3 %collective-permute-start.50 = (f32[2,16,512]{2,1,0:T(8,128)S(1)}, f32[2,16,512]{2,1,0:T(8,128)S(1)}, u32[]{:S(2)}, u32[]{:S(2)}) collective-permute-start(f32[2,16,512]{2,1,0:T(8,128)S(1)} %get-tuple-element.83), channel_id=1, source_target_pairs={{0,16},{4,20},{8,24},{12,28},{16,0},{20,4},{24,8},{28,12},{1,17},{... | collective-permute-start | bytes 196616 | tf_op jit(solution)/shard_map/ppermute | solution.py:81
  106.0 4.3 %collective-permute-start.51 = (f32[2,16,512]{2,1,0:T(8,128)S(1)}, f32[2,16,512]{2,1,0:T(8,128)S(1)}, u32[]{:S(2)}, u32[]{:S(2)}) collective-permute-start(f32[2,16,512]{2,1,0:T(8,128)S(1)} %get-tuple-element.84), channel_id=1, source_target_pairs={{0,8},{4,12},{8,0},{12,4},{16,24},{20,28},{24,16},{28,20},{1,9},{5... | collective-permute-start | bytes 196616 | tf_op jit(solution)/shard_map/ppermute | solution.py:81
  110.7 7.7 %collective-permute-start.52 = (f32[16,1280]{1,0:T(8,128)S(1)}, f32[16,1280]{1,0:T(8,128)S(1)}, u32[]{:S(2)}, u32[]{:S(2)}) collective-permute-start(f32[16,1280]{1,0:T(8,128)S(1)} %get-tuple-element.87), channel_id=1, source_target_pairs={{0,2},{1,3},{2,0},{3,1},{4,6},{5,7},{6,4},{7,5},{8,10},{9,11},{10,... | collective-permute-start | bytes 245768 | tf_op jit(solution)/shard_map/ppermute | solution.py:33
  111.7 6.7 %collective-permute-start.53 = (f32[16,1280]{1,0:T(8,128)S(1)}, f32[16,1280]{1,0:T(8,128)S(1)}, u32[]{:S(2)}, u32[]{:S(2)}) collective-permute-start(f32[16,1280]{1,0:T(8,128)S(1)} %get-tuple-element.88), channel_id=1, source_target_pairs={{0,3},{1,2},{2,1},{3,0},{4,7},{5,6},{6,5},{7,4},{8,11},{9,10},{10,... | collective-permute-start | bytes 245768 | tf_op jit(solution)/shard_map/ppermute | solution.py:33
  113.1 6.0 %collective-permute-start.54 = (f32[16,1280]{1,0:T(8,128)S(1)}, f32[16,1280]{1,0:T(8,128)S(1)}, u32[]{:S(2)}, u32[]{:S(2)}) collective-permute-start(f32[16,1280]{1,0:T(8,128)S(1)} %get-tuple-element.89), channel_id=1, source_target_pairs={{0,1},{1,0},{2,3},{3,2},{4,5},{5,4},{6,7},{7,6},{8,9},{9,8},{10,11... | collective-permute-start | bytes 245768 | tf_op jit(solution)/shard_map/ppermute | solution.py:33
  119.5 4.7 %collective-permute-start.55 = (f32[16,256]{1,0:T(8,128)S(1)}, f32[16,256]{1,0:T(8,128)S(1)}, u32[]{:S(2)}, u32[]{:S(2)}) collective-permute-start(f32[16,256]{1,0:T(8,128)S(1)} %get-tuple-element.92.refs_0_.refs_6_), channel_id=1, source_target_pairs={{0,2},{1,3},{2,0},{3,1},{4,6},{5,7},{6,4},{7,5},{8,10},{9,11},{10,... | collective-permute-start | bytes 49160 | tf_op jit(solution)/shard_map/ppermute | solution.py:33
  121.1 5.5 %collective-permute-start.56 = (f32[16,256]{1,0:T(8,128)S(1)}, f32[16,256]{1,0:T(8,128)S(1)}, u32[]{:S(2)}, u32[]{:S(2)}) collective-permute-start(f32[16,256]{1,0:T(8,128)S(1)} %get-tuple-element.92.refs_0_.refs_6_), channel_id=1, source_target_pairs={{0,3},{1,2},{2,1},{3,0},{4,7},{5,6},{6,5},{7,4},{8,11},{9,10},{10,... | collective-permute-start | bytes 49160 | tf_op jit(solution)/shard_map/ppermute | solution.py:33
  122.5 4.1 %collective-permute-start.57 = (f32[16,256]{1,0:T(8,128)S(1)}, f32[16,256]{1,0:T(8,128)S(1)}, u32[]{:S(2)}, u32[]{:S(2)}) collective-permute-start(f32[16,256]{1,0:T(8,128)S(1)} %get-tuple-element.92.refs_0_.refs_6_), channel_id=1, source_target_pairs={{0,1},{1,0},{2,3},{3,2},{4,5},{5,4},{6,7},{7,6},{8,9},{9,8},{10,11... | collective-permute-start | bytes 49160 | tf_op jit(solution)/shard_map/ppermute | solution.py:33
  127.0 4.7 %collective-permute-start.58 = (f32[16,256]{1,0:T(8,128)S(1)}, f32[16,256]{1,0:T(8,128)S(1)}, u32[]{:S(2)}, u32[]{:S(2)}) collective-permute-start(f32[16,256]{1,0:T(8,128)S(1)} %shard_map.124.refs_0_), channel_id=1, source_target_pairs={{0,2},{1,3},{2,0},{3,1},{4,6},{5,7},{6,4},{7,5},{8,10},{9,11},{10,... | collective-permute-start | bytes 49160 | tf_op jit(solution)/shard_map/ppermute | solution.py:33
  127.8 5.6 %collective-permute-start.59 = (f32[16,256]{1,0:T(8,128)S(1)}, f32[16,256]{1,0:T(8,128)S(1)}, u32[]{:S(2)}, u32[]{:S(2)}) collective-permute-start(f32[16,256]{1,0:T(8,128)S(1)} %shard_map.124.refs_0_), channel_id=1, source_target_pairs={{0,3},{1,2},{2,1},{3,0},{4,7},{5,6},{6,5},{7,4},{8,11},{9,10},{10,... | collective-permute-start | bytes 49160 | tf_op jit(solution)/shard_map/ppermute | solution.py:33
  129.5 3.9 %collective-permute-start.60 = (f32[16,256]{1,0:T(8,128)S(1)}, f32[16,256]{1,0:T(8,128)S(1)}, u32[]{:S(2)}, u32[]{:S(2)}) collective-permute-start(f32[16,256]{1,0:T(8,128)S(1)} %shard_map.124.refs_0_), channel_id=1, source_target_pairs={{0,1},{1,0},{2,3},{3,2},{4,5},{5,4},{6,7},{7,6},{8,9},{9,8},{10,11... | collective-permute-start | bytes 49160 | tf_op jit(solution)/shard_map/ppermute | solution.py:33
  (7 other events, 95.4 us)

commit v21 on v20

--- a/solution.py
+++ b/solution.py
@@ -247,6 +247,7 @@
         [rhs],
         [ANY],
         scratch=[pltpu.VMEM((rows, count), jnp.float32), pltpu.SemaphoreType.DMA(())],
+        limit=121 * 2**19,
     )
 
 
@@ -298,7 +299,7 @@
     ancestors, part, rows = rhs_turned.shape
     inner = received[0].shape[0]
     block_count = ancestors * order // tile_rows
-    width = order + (ancestors - 1) * rows
+    width = (ancestors - 1) * rows
 
     def body(*refs):
         sources = refs[: len(received)]
@@ -321,20 +322,20 @@
             for j in range(members):
                 at = slice(a * order + j * rows, a * order + (j + 1) * rows)
                 share[:, at] = share[:, at] + jnp.where(me == j, rhs_ref[a], 0.0)
+        outs[0][...] = share[:, :order]
         for distance in range(members):
             target = partner(me, -distance, members) if distance else me
-            out = outs[distance]
-            out[:, :order] = share[:, :order]
+            out = outs[1 + distance]
             for a in range(1, ancestors):
                 value = jnp.zeros((part, rows), jnp.float32)
                 for j in range(members):
                     at = slice(a * order + j * rows, a * order + (j + 1) * rows)
                     value = jnp.where(target == j, share[:, at], value)
-                out[:, order + (a - 1) * rows : order + a * rows] = value
-
-    return local_kernel(
-        body,
-        [float_array(part, width)] * members,
+                out[:, (a - 1) * rows : a * rows] = value
+
+    return local_kernel(
+        body,
+        [float_array(part, order)] + [float_array(part, width)] * members,
         [*received, rhs_turned, after],
         [VMEM] * (len(received) + 1) + [ANY],
         scratch=[pltpu.VMEM((part, ancestors * order), jnp.float32)],
@@ -362,24 +363,55 @@
     )
 
 
-def solve_first(payloads, top, rest):
-    part, width = payloads[0].shape
+def solve_first(shares, others, top, rest):
+    members = len(others)
+    part, width = others[0].shape
     rows, order = top.shape[1:]
 
     def body(*refs):
-        sums = refs[: len(payloads)]
-        top_ref, rest_ref, out, left = refs[len(payloads) :]
-        total = sums[0][...]
-        for ref in sums[1:]:
+        total = refs[0][...]
+        for ref in refs[1:members]:
             total = total + ref[...]
-        out[...] = split_product(total[:, :order], top_ref[0], rest_ref[0])
-        left[...] = total[:, order:]
-
-    return local_kernel(
-        body,
-        [float_array(part, rows), float_array(part, width - order)],
-        [*payloads, top, rest],
+        other_refs = refs[members : 2 * members]
+        top_ref, rest_ref, out = refs[2 * members : 2 * members + 3]
+        value = split_product(total, top_ref[0], rest_ref[0])
+        out[...] = value
+        for distance in range(1, members):
+            message = refs[2 * members + 2 + distance]
+            message[:, :rows] = value
+            message[:, rows:] = other_refs[distance][...]
+
+    return local_kernel(
+        body,
+        [float_array(part, rows)] + [float_array(part, rows + width)] * (members - 1),
+        [*shares, *others, top, rest],
         flops=6 * part * rows * order,
+    )
+
+
+def take_messages(own, other, messages, top, rest):
+    members = len(messages) + 1
+    part, width = other.shape
+    rows, order = top.shape[1:]
+
+    def body(*refs):
+        own_ref, other_ref = refs[:2]
+        held = refs[2 : members + 1]
+        top_ref, rest_ref, out, left, whole = refs[members + 1 :]
+        total = other_ref[...]
+        for ref in held:
+            total = total + ref[:, rows:]
+        left[...] = total
+        pieces = [ref[:, :rows] for ref in held[-1:] + held[:-1]]
+        put_in_order([own_ref[...]] + pieces, whole)
+        out[...] = total[:, :rows] - split_product(whole[...], top_ref[0], rest_ref[0])
+
+    return local_kernel(
+        body,
+        [float_array(part, rows), float_array(part, width)],
+        [own, other, *messages, top, rest],
+        flops=6 * part * rows * order,
+        scratch=[pltpu.VMEM((part, order), jnp.float32)],
     )
 
 
@@ -497,21 +529,26 @@
         received, jnp.swapaxes(rhs_anc, 1, 2), order, slots, tile_rows, tie
     )
     far_first = list(range(2, members)) + list(range(1, min(members, 2)))
-    payloads = [shares[0]] + [send(shares[d], "grp", d) for d in far_first]
+    first_share, others = shares[0], shares[1:]
+    sums = [first_share] + [send(first_share, "grp", d) for d in far_first]
     inverse_top, inverse_rest, below_top, below_rest = split_factors(
-        [diag_inv_anc, sub_anc], shares[0]
-    )
-    solution, left = solve_first(payloads, inverse_top, inverse_rest)
+        [diag_inv_anc, sub_anc], first_share
+    )
+    solution, *messages = solve_first(sums, others, inverse_top, inverse_rest)
     solutions = [solution]
     ancestors = rhs_anc.shape[0]
     for ancestor in range(1, ancestors):
-        pieces = gather_far_first(solutions[-1])
-        residual = apply_split(
-            pieces, below_top, below_rest, ancestor - 1, left, (ancestor - 1) * rows
-        )
+        if ancestor == 1:
+            arrived = [send(messages[d - 1], "grp", d) for d in far_first]
+            residual, left = take_messages(solution, others[0], arrived, below_top, below_rest)
+        else:
+            pieces = gather_far_first(solutions[-1])
+            residual = apply_split(
+                pieces, below_top, below_rest, ancestor - 1, left, (ancestor - 1) * rows
+            )
         pieces = gather_far_first(residual)
-        others = solutions if ancestor + 1 == ancestors else None
-        solved_now = apply_split(pieces, inverse_top, inverse_rest, ancestor, others=others)
+        behind = solutions if ancestor + 1 == ancestors else None
+        solved_now = apply_split(pieces, inverse_top, inverse_rest, ancestor, others=behind)
         solutions.append(solved_now)
     solutions = solutions[-1] if ancestors > 1 else solutions[0][None]
     solutions = jnp.swapaxes(solutions, 1, 2)

time: 135 us -> 136 us (level)
  starting transfers between devices: 90.2 us -> 85.9 us
  waiting for transfers between devices: 23.8 us -> 27.7 us
  Pallas kernels: 7.53 us -> 9.58 us
    ppermute x57, starting transfers between devices: 86.6 us -> 82.1 us  [send(): return lax.ppermute(value, axis, pairs)]
    ppermute x57, waiting for transfers between devices: 19.7 us -> 23.8 us  [send(): return lax.ppermute(value, axis, pairs)]
    pallas_call x13, Pallas kernels: 7.53 us -> 9.58 us  [local_kernel(): pl.pallas_call(body, out_shape=list(outs), in_specs=specs or [VMEM] * len...]
  transfers between devices with their start and end apart: 61 -> 61, of which waited for: 17 -> 27; matrix products, arithmetic and copies ran while one was open for 7% -> 7% of each run, Pallas kernels for 3% -> 3%
where the time goes in v21:
time: 136 us
  starting transfers between devices  85.9 us (63%)
  waiting for transfers between devices  27.7 us (20%)
  Pallas kernels  9.58 us (7%)
  matrix products  7.59 us (6%)
  between operations  2 us (1%)
  local copies, waits for them, and re-layouts  1.62 us (1%)
  other arithmetic  1.41 us (1%)
    ppermute x57, starting transfers between devices, send(): return lax.ppermute(value, axis, pairs)  82.1 us
    ppermute x57, waiting for transfers between devices, send(): return lax.ppermute(value, axis, pairs)  23.8 us
    pallas_call x13, Pallas kernels, local_kernel(): pl.pallas_call(body, out_shape=list(outs), in_specs=specs or [VMEM] * len...  9.58 us
    dot_general x12, matrix products, contract_last(): lax.dot_general(left, right, (((left.ndim - 1,), (right.ndim - 1,)), ((),...  7.59 us
    ppermute x3, starting transfers between devices, swap(): return lax.ppermute(value, axis, pairs)  3.77 us
  transfers between devices with their start and end apart: 61, of which 27 were waited for; matrix products, arithmetic and copies ran while one was open for 7% of the time, Pallas kernels for 3%

profile of v21, /device:TPU:0, one launch (start us, length us, event | category | flops | bytes accessed | tf_op | source)
XLA Modules:
  0.0 135.9 jit_solution(12165296930890142674)
XLA Ops:
  0.6 1.7 %shard_map.113 = (f32[64,256]{1,0:T(8,128)}, f32[64,256]{1,0:T(8,128)}) custom-call(f32[1,4,256,128]{3,2,1,0:T(8,128)} %rhs_ref.3), custom_call_target="tpu_custom_call" | custom-call | bytes 655360 | tf_op jit(solution)/shard_map/pallas_call | solution.py:91
  2.4 3.1 %collective-permute-start = (f32[64,256]{1,0:T(8,128)}, f32[64,256]{1,0:T(8,128)S(1)}, u32[]{:S(2)}, u32[]{:S(2)}) collective-permute-start(f32[64,256]{1,0:T(8,128)} %get-tuple-element.53.refs_0_), channel_id=1, source_target_pairs={{0,1},{1,0},{2,3},{3,2},{4,5},{5,4},{6,7},{7,6},{8,9},{9,8},{10,11... | collective-permute-start | bytes 196616 | tf_op jit(solution)/shard_map/ppermute | solution.py:33
  5.5 2.6 %collective-permute-start.1 = (f32[64,256]{1,0:T(8,128)}, f32[64,256]{1,0:T(8,128)S(1)}, u32[]{:S(2)}, u32[]{:S(2)}) collective-permute-start(f32[64,256]{1,0:T(8,128)} %get-tuple-element.53.refs_0_), channel_id=1, source_target_pairs={{0,2},{1,3},{2,0},{3,1},{4,6},{5,7},{6,4},{7,5},{8,10},{9,11},{10,... | collective-permute-start | bytes 196616 | tf_op jit(solution)/shard_map/ppermute | solution.py:33
  8.0 0.9 collective-permute-start.3
  8.9 3.5 %collective-permute-start.4 = (f32[64,256]{1,0:T(8,128)}, f32[64,256]{1,0:T(8,128)S(1)}, u32[]{:S(2)}, u32[]{:S(2)}) collective-permute-start(f32[64,256]{1,0:T(8,128)} %get-tuple-element.54.refs_0_), channel_id=1, source_target_pairs={{0,2},{1,3},{2,0},{3,1},{4,6},{5,7},{6,4},{7,5},{8,10},{9,11},{10,... | collective-permute-start | bytes 196616 | tf_op jit(solution)/shard_map/ppermute | solution.py:33
  12.6 1.4 %fusion = (bf16[1,256,1024]{2,1,0:T(8,128)(2,1)S(1)}, bf16[1,256,1024]{2,1,0:T(8,128)(2,1)S(1)}) fusion(f32[1,4,256,1024]{3,2,1,0:T(8,128)} %param.11), kind=kLoop, calls=%fused_computation.2 | loop fusion | flops 1048576 | bytes 2097152 | tf_op jit(solution)/shard_map/convert_element_type | solution.py:486
  14.8 0.8 copy-done.5
  16.1 3.3 %collective-permute-start.6 = (f32[64,256]{1,0:T(8,128)S(1)}, f32[64,256]{1,0:T(8,128)S(1)}, u32[]{:S(2)}, u32[]{:S(2)}) collective-permute-start(f32[64,256]{1,0:T(8,128)S(1)} %shard_map.114.refs_0_), channel_id=1, source_target_pairs={{0,1},{1,0},{2,3},{3,2},{4,5},{5,4},{6,7},{7,6},{8,9},{9,8},{10,11... | collective-permute-start | bytes 196616 | tf_op jit(solution)/shard_map/ppermute | solution.py:33
  19.4 1.9 %collective-permute-start.7 = (f32[64,256]{1,0:T(8,128)S(1)}, f32[64,256]{1,0:T(8,128)S(1)}, u32[]{:S(2)}, u32[]{:S(2)}) collective-permute-start(f32[64,256]{1,0:T(8,128)S(1)} %shard_map.114.refs_0_), channel_id=1, source_target_pairs={{0,2},{1,3},{2,0},{3,1},{4,6},{5,7},{6,4},{7,5},{8,10},{9,11},{10,... | collective-permute-start | bytes 196616 | tf_op jit(solution)/shard_map/ppermute | solution.py:33
  21.3 1.4 %collective-permute-start.8 = (f32[64,256]{1,0:T(8,128)S(1)}, f32[64,256]{1,0:T(8,128)S(1)}, u32[]{:S(2)}, u32[]{:S(2)}) collective-permute-start(f32[64,256]{1,0:T(8,128)S(1)} %shard_map.114.refs_0_), channel_id=1, source_target_pairs={{0,3},{1,2},{2,1},{3,0},{4,7},{5,6},{6,5},{7,4},{8,11},{9,10},{10,... | collective-permute-start | bytes 196616 | tf_op jit(solution)/shard_map/ppermute | solution.py:33
  23.2 2.1 %collective-permute-start.9 = (f32[64,256]{1,0:T(8,128)S(1)}, f32[64,256]{1,0:T(8,128)S(1)}, u32[]{:S(2)}, u32[]{:S(2)}) collective-permute-start(f32[64,256]{1,0:T(8,128)S(1)} %shard_map.115.refs_1_), channel_id=1, source_target_pairs={{0,2},{1,3},{2,0},{3,1},{4,6},{5,7},{6,4},{7,5},{8,10},{9,11},{10,... | collective-permute-start | bytes 196616 | tf_op jit(solution)/shard_map/ppermute | solution.py:33
  25.3 0.9 collective-permute-start.13
  28.5 6.3 %collective-permute-start.11 = (f32[64,256]{1,0:T(8,128)S(1)}, f32[64,256]{1,0:T(8,128)S(1)}, u32[]{:S(2)}, u32[]{:S(2)}) collective-permute-start(f32[64,256]{1,0:T(8,128)S(1)} %get-tuple-element.57), channel_id=1, source_target_pairs={{0,2},{1,3},{2,0},{3,1},{4,6},{5,7},{6,4},{7,5},{8,10},{9,11},{10,... | collective-permute-start | bytes 196616 | tf_op jit(solution)/shard_map/ppermute | solution.py:33
  36.1 3.8 %collective-permute-start.16 = (f32[64,256]{1,0:T(8,128)S(1)}, f32[64,256]{1,0:T(8,128)S(1)}, u32[]{:S(2)}, u32[]{:S(2)}) collective-permute-start(f32[64,256]{1,0:T(8,128)S(1)} %get-tuple-element.60), channel_id=1, source_target_pairs={{0,2},{1,3},{2,0},{3,1},{4,6},{5,7},{6,4},{7,5},{8,10},{9,11},{10,... | collective-permute-start | bytes 196616 | tf_op jit(solution)/shard_map/ppermute | solution.py:33
  41.7 3.5 %collective-permute-start.19 = (f32[64,256]{1,0:T(8,128)S(1)}, f32[64,256]{1,0:T(8,128)S(1)}, u32[]{:S(2)}, u32[]{:S(2)}) collective-permute-start(f32[64,256]{1,0:T(8,128)S(1)} %get-tuple-element.62.refs_2_), channel_id=1, source_target_pairs={{0,2},{1,3},{2,0},{3,1},{4,6},{5,7},{6,4},{7,5},{8,10},{9,11},{10,... | collective-permute-start | bytes 196616 | tf_op jit(solution)/shard_map/ppermute | solution.py:33
  45.8 1.5 %collective-permute-done.15 = f32[64,256]{1,0:T(8,128)S(1)} collective-permute-done((f32[64,256]{1,0:T(8,128)S(1)}, f32[64,256]{1,0:T(8,128)S(1)}, u32[]{:S(2)}, u32[]{:S(2)}) %collective-permute-start.15) | collective-permute-done | bytes 65568 | tf_op jit(solution)/shard_map/ppermute | solution.py:33
  48.0 2.3 %collective-permute-start.21 = (f32[64,256]{1,0:T(8,128)S(1)}, f32[64,256]{1,0:T(8,128)S(1)}, u32[]{:S(2)}, u32[]{:S(2)}) collective-permute-start(f32[64,256]{1,0:T(8,128)S(1)} %get-tuple-element.66.refs_3_), channel_id=1, source_target_pairs={{0,2},{1,3},{2,0},{3,1},{4,6},{5,7},{6,4},{7,5},{8,10},{9,11},{10,... | collective-permute-start | bytes 196616 | tf_op jit(solution)/shard_map/ppermute | solution.py:33
  50.3 1.4 %collective-permute-start.25 = (f32[64,256]{1,0:T(8,128)S(1)}, f32[64,256]{1,0:T(8,128)S(1)}, u32[]{:S(2)}, u32[]{:S(2)}) collective-permute-start(f32[64,256]{1,0:T(8,128)S(1)} %get-tuple-element.66.refs_3_), channel_id=1, source_target_pairs={{0,3},{1,2},{2,1},{3,0},{4,7},{5,6},{6,5},{7,4},{8,11},{9,10},{10,... | collective-permute-start | bytes 196616 | tf_op jit(solution)/shard_map/ppermute | solution.py:33
  52.5 3.0 %collective-permute-start.23 = (f32[64,256]{1,0:T(8,128)S(1)}, f32[64,256]{1,0:T(8,128)S(1)}, u32[]{:S(2)}, u32[]{:S(2)}) collective-permute-start(f32[64,256]{1,0:T(8,128)S(1)} %get-tuple-element.65), channel_id=1, source_target_pairs={{0,2},{1,3},{2,0},{3,1},{4,6},{5,7},{6,4},{7,5},{8,10},{9,11},{10,... | collective-permute-start | bytes 196616 | tf_op jit(solution)/shard_map/ppermute | solution.py:33
  55.5 1.9 %collective-permute-start.26 = (f32[64,256]{1,0:T(8,128)S(1)}, f32[64,256]{1,0:T(8,128)S(1)}, u32[]{:S(2)}, u32[]{:S(2)}) collective-permute-start(f32[64,256]{1,0:T(8,128)S(1)} %get-tuple-element.65), channel_id=1, source_target_pairs={{0,3},{1,2},{2,1},{3,0},{4,7},{5,6},{6,5},{7,4},{8,11},{9,10},{10,... | collective-permute-start | bytes 196616 | tf_op jit(solution)/shard_map/ppermute | solution.py:33
  57.4 1.5 %collective-permute-done.24 = f32[64,256]{1,0:T(8,128)S(1)} collective-permute-done((f32[64,256]{1,0:T(8,128)S(1)}, f32[64,256]{1,0:T(8,128)S(1)}, u32[]{:S(2)}, u32[]{:S(2)}) %collective-permute-start.24) | collective-permute-done | bytes 65568 | tf_op jit(solution)/shard_map/ppermute | solution.py:33
  59.7 2.3 %collective-permute-start.28 = (f32[64,256]{1,0:T(8,128)S(1)}, f32[64,256]{1,0:T(8,128)S(1)}, u32[]{:S(2)}, u32[]{:S(2)}) collective-permute-start(f32[64,256]{1,0:T(8,128)S(1)} %get-tuple-element.68), channel_id=1, source_target_pairs={{0,2},{1,3},{2,0},{3,1},{4,6},{5,7},{6,4},{7,5},{8,10},{9,11},{10,... | collective-permute-start | bytes 196616 | tf_op jit(solution)/shard_map/ppermute | solution.py:33
  61.9 2.3 %collective-permute-start.29 = (f32[64,256]{1,0:T(8,128)S(1)}, f32[64,256]{1,0:T(8,128)S(1)}, u32[]{:S(2)}, u32[]{:S(2)}) collective-permute-start(f32[64,256]{1,0:T(8,128)S(1)} %get-tuple-element.68), channel_id=1, source_target_pairs={{0,3},{1,2},{2,1},{3,0},{4,7},{5,6},{6,5},{7,4},{8,11},{9,10},{10,... | collective-permute-start | bytes 196616 | tf_op jit(solution)/shard_map/ppermute | solution.py:33
  64.2 0.8 collective-permute-done.22
  65.8 1.3 collective-permute-start.31
  67.1 2.3 %collective-permute-start.32 = (f32[64,256]{1,0:T(8,128)S(1)}, f32[64,256]{1,0:T(8,128)S(1)}, u32[]{:S(2)}, u32[]{:S(2)}) collective-permute-start(f32[64,256]{1,0:T(8,128)S(1)} %get-tuple-element.70.refs_4_), channel_id=1, source_target_pairs={{0,3},{1,2},{2,1},{3,0},{4,7},{5,6},{6,5},{7,4},{8,11},{9,10},{10,... | collective-permute-start | bytes 196616 | tf_op jit(solution)/shard_map/ppermute | solution.py:33
  69.4 1.6 %collective-permute-done.27 = f32[64,256]{1,0:T(8,128)S(1)} collective-permute-done((f32[64,256]{1,0:T(8,128)S(1)}, f32[64,256]{1,0:T(8,128)S(1)}, u32[]{:S(2)}, u32[]{:S(2)}) %collective-permute-start.27) | collective-permute-done | bytes 65568 | tf_op jit(solution)/shard_map/ppermute | solution.py:33
  71.7 1.6 %collective-permute-start.33 = (f32[64,256]{1,0:T(8,128)S(1)}, f32[64,256]{1,0:T(8,128)S(1)}, u32[]{:S(2)}, u32[]{:S(2)}) collective-permute-start(f32[64,256]{1,0:T(8,128)S(1)} %get-tuple-element.74.refs_5_), channel_id=1, source_target_pairs={{0,2},{1,3},{2,0},{3,1},{4,6},{5,7},{6,4},{7,5},{8,10},{9,11},{10,... | collective-permute-start | bytes 196616 | tf_op jit(solution)/shard_map/ppermute | solution.py:33
  73.2 1.3 collective-permute-start.37
  75.2 0.9 collective-permute-done.30
  76.9 1.5 %collective-permute-start.35 = (f32[64,256]{1,0:T(8,128)S(1)}, f32[64,256]{1,0:T(8,128)S(1)}, u32[]{:S(2)}, u32[]{:S(2)}) collective-permute-start(f32[64,256]{1,0:T(8,128)S(1)} %get-tuple-element.73), channel_id=1, source_target_pairs={{0,2},{1,3},{2,0},{3,1},{4,6},{5,7},{6,4},{7,5},{8,10},{9,11},{10,... | collective-permute-start | bytes 196616 | tf_op jit(solution)/shard_map/ppermute | solution.py:33
  78.4 1.4 %collective-permute-start.38 = (f32[64,256]{1,0:T(8,128)S(1)}, f32[64,256]{1,0:T(8,128)S(1)}, u32[]{:S(2)}, u32[]{:S(2)}) collective-permute-start(f32[64,256]{1,0:T(8,128)S(1)} %get-tuple-element.73), channel_id=1, source_target_pairs={{0,3},{1,2},{2,1},{3,0},{4,7},{5,6},{6,5},{7,4},{8,11},{9,10},{10,... | collective-permute-start | bytes 196616 | tf_op jit(solution)/shard_map/ppermute | solution.py:33
  80.5 1.4 %collective-permute-done.36 = f32[64,256]{1,0:T(8,128)S(1)} collective-permute-done((f32[64,256]{1,0:T(8,128)S(1)}, f32[64,256]{1,0:T(8,128)S(1)}, u32[]{:S(2)}, u32[]{:S(2)}) %collective-permute-start.36) | collective-permute-done | bytes 65568 | tf_op jit(solution)/shard_map/ppermute | solution.py:33
  82.6 1.9 %collective-permute-start.40 = (f32[64,256]{1,0:T(8,128)S(1)}, f32[64,256]{1,0:T(8,128)S(1)}, u32[]{:S(2)}, u32[]{:S(2)}) collective-permute-start(f32[64,256]{1,0:T(8,128)S(1)} %get-tuple-element.76), channel_id=1, source_target_pairs={{0,2},{1,3},{2,0},{3,1},{4,6},{5,7},{6,4},{7,5},{8,10},{9,11},{10,... | collective-permute-start | bytes 196616 | tf_op jit(solution)/shard_map/ppermute | solution.py:33
  84.5 2.5 %collective-permute-start.41 = (f32[64,256]{1,0:T(8,128)S(1)}, f32[64,256]{1,0:T(8,128)S(1)}, u32[]{:S(2)}, u32[]{:S(2)}) collective-permute-start(f32[64,256]{1,0:T(8,128)S(1)} %get-tuple-element.76), channel_id=1, source_target_pairs={{0,3},{1,2},{2,1},{3,0},{4,7},{5,6},{6,5},{7,4},{8,11},{9,10},{10,... | collective-permute-start | bytes 196616 | tf_op jit(solution)/shard_map/ppermute | solution.py:33
  88.2 1.4 %collective-permute-start.43 = (f32[64,256]{1,0:T(8,128)S(1)}, f32[64,256]{1,0:T(8,128)S(1)}, u32[]{:S(2)}, u32[]{:S(2)}) collective-permute-start(f32[64,256]{1,0:T(8,128)S(1)} %get-tuple-element.78.refs_6_), channel_id=1, source_target_pairs={{0,2},{1,3},{2,0},{3,1},{4,6},{5,7},{6,4},{7,5},{8,10},{9,11},{10,... | collective-permute-start | bytes 196616 | tf_op jit(solution)/shard_map/ppermute | solution.py:33
  89.7 2.5 %collective-permute-start.44 = (f32[64,256]{1,0:T(8,128)S(1)}, f32[64,256]{1,0:T(8,128)S(1)}, u32[]{:S(2)}, u32[]{:S(2)}) collective-permute-start(f32[64,256]{1,0:T(8,128)S(1)} %get-tuple-element.78.refs_6_), channel_id=1, source_target_pairs={{0,3},{1,2},{2,1},{3,0},{4,7},{5,6},{6,5},{7,4},{8,11},{9,10},{10,... | collective-permute-start | bytes 196616 | tf_op jit(solution)/shard_map/ppermute | solution.py:33
  92.2 1.5 %collective-permute-done.39 = f32[64,256]{1,0:T(8,128)S(1)} collective-permute-done((f32[64,256]{1,0:T(8,128)S(1)}, f32[64,256]{1,0:T(8,128)S(1)}, u32[]{:S(2)}, u32[]{:S(2)}) %collective-permute-start.39) | collective-permute-done | bytes 65568 | tf_op jit(solution)/shard_map/ppermute | solution.py:33
  95.0 2.4 %collective-permute-start.47 = (f32[64,256]{1,0:T(8,128)S(1)}, f32[64,256]{1,0:T(8,128)S(1)}, u32[]{:S(2)}, u32[]{:S(2)}) collective-permute-start(f32[64,256]{1,0:T(8,128)S(1)} %get-tuple-element.80.refs_7_), channel_id=1, source_target_pairs={{0,3},{1,2},{2,1},{3,0},{4,7},{5,6},{6,5},{7,4},{8,11},{9,10},{10,... | collective-permute-start | bytes 196616 | tf_op jit(solution)/shard_map/ppermute | solution.py:33
  97.4 0.6 collective-permute-start.45
  98.1 2.2 %collective-permute-done.46 = f32[64,256]{1,0:T(8,128)S(1)} collective-permute-done((f32[64,256]{1,0:T(8,128)S(1)}, f32[64,256]{1,0:T(8,128)S(1)}, u32[]{:S(2)}, u32[]{:S(2)}) %collective-permute-start.46) | collective-permute-done | bytes 65568 | tf_op jit(solution)/shard_map/ppermute | solution.py:33
  100.3 1.2 shard_map.117.refs_0_
  102.0 1.2 shard_map.118
  103.3 1.3 collective-permute-done.48.refs_1_
  104.6 3.1 %collective-permute-start.49 = (f32[2,16,512]{2,1,0:T(8,128)S(1)}, f32[2,16,512]{2,1,0:T(8,128)S(1)}, u32[]{:S(2)}, u32[]{:S(2)}) collective-permute-start(f32[2,16,512]{2,1,0:T(8,128)S(1)} %get-tuple-element.86), channel_id=1, source_target_pairs={{0,24},{4,28},{8,16},{12,20},{16,8},{20,12},{24,0},{28,4},{1,25},{... | collective-permute-start | bytes 196616 | tf_op jit(solution)/shard_map/ppermute | solution.py:81
  108.4 1.0 shard_map.119
  109.4 0.8 collective-permute-done.49.refs_1_
  110.2 1.9 %collective-permute-done.50.refs_2_ = f32[2,16,512]{2,1,0:T(8,128)S(1)} collective-permute-done((f32[2,16,512]{2,1,0:T(8,128)S(1)}, f32[2,16,512]{2,1,0:T(8,128)S(1)}, u32[]{:S(2)}, u32[]{:S(2)}) %collective-permute-start.50) | collective-permute-done | bytes 65568 | tf_op jit(solution)/shard_map/ppermute | solution.py:81
  112.4 1.0 collective-permute-start.52
  113.4 1.4 %collective-permute-start.53 = (f32[16,1024]{1,0:T(8,128)S(1)}, f32[16,1024]{1,0:T(8,128)S(1)}, u32[]{:S(2)}, u32[]{:S(2)}) collective-permute-start(f32[16,1024]{1,0:T(8,128)S(1)} %get-tuple-element.90.refs_2_.refs_0_), channel_id=1, source_target_pairs={{0,3},{1,2},{2,1},{3,0},{4,7},{5,6},{6,5},{7,4},{8,11},{9,10},{10,... | collective-permute-start | bytes 196616 | tf_op jit(solution)/shard_map/ppermute | solution.py:33
  114.8 1.1 collective-permute-start.54
  116.5 2.0 %collective-permute-done.52.refs_1_ = f32[16,1024]{1,0:T(8,128)S(1)} collective-permute-done((f32[16,1024]{1,0:T(8,128)S(1)}, f32[16,1024]{1,0:T(8,128)S(1)}, u32[]{:S(2)}, u32[]{:S(2)}) %collective-permute-start.52) | collective-permute-done | bytes 65568 | tf_op jit(solution)/shard_map/ppermute | solution.py:33
  118.5 1.2 collective-permute-done.53.refs_2_
  120.3 1.1 collective-permute-start.55
  121.4 1.9 %collective-permute-start.56 = (f32[16,512]{1,0:T(8,128)S(1)}, f32[16,512]{1,0:T(8,128)S(1)}, u32[]{:S(2)}, u32[]{:S(2)}) collective-permute-start(f32[16,512]{1,0:T(8,128)S(1)} %get-tuple-element.99), channel_id=1, source_target_pairs={{0,3},{1,2},{2,1},{3,0},{4,7},{5,6},{6,5},{7,4},{8,11},{9,10},{10,... | collective-permute-start | bytes 98312 | tf_op jit(solution)/shard_map/ppermute | solution.py:33
  123.8 1.7 %collective-permute-done.55.refs_2_ = f32[16,512]{1,0:T(8,128)S(1)} collective-permute-done((f32[16,512]{1,0:T(8,128)S(1)}, f32[16,512]{1,0:T(8,128)S(1)}, u32[]{:S(2)}, u32[]{:S(2)}) %collective-permute-start.55) | collective-permute-done | bytes 32800 | tf_op jit(solution)/shard_map/ppermute | solution.py:33
  125.5 1.7 %collective-permute-done.56.refs_3_ = f32[16,512]{1,0:T(8,128)S(1)} collective-permute-done((f32[16,512]{1,0:T(8,128)S(1)}, f32[16,512]{1,0:T(8,128)S(1)}, u32[]{:S(2)}, u32[]{:S(2)}) %collective-permute-start.56) | collective-permute-done | bytes 32800 | tf_op jit(solution)/shard_map/ppermute | solution.py:33
  127.5 0.9 shard_map.124
  128.3 0.8 collective-permute-start.58
  129.1 1.9 %collective-permute-start.59 = (f32[16,256]{1,0:T(8,128)S(1)}, f32[16,256]{1,0:T(8,128)S(1)}, u32[]{:S(2)}, u32[]{:S(2)}) collective-permute-start(f32[16,256]{1,0:T(8,128)S(1)} %get-tuple-element.103.refs_0_), channel_id=1, source_target_pairs={{0,3},{1,2},{2,1},{3,0},{4,7},{5,6},{6,5},{7,4},{8,11},{9,10},{10,... | collective-permute-start | bytes 49160 | tf_op jit(solution)/shard_map/ppermute | solution.py:33
  131.0 0.9 collective-permute-start.60
  131.8 1.1 collective-permute-done.58.refs_1_
  133.0 1.7 %collective-permute-done.59.refs_2_ = f32[16,256]{1,0:T(8,128)S(1)} collective-permute-done((f32[16,256]{1,0:T(8,128)S(1)}, f32[16,256]{1,0:T(8,128)S(1)}, u32[]{:S(2)}, u32[]{:S(2)}) %collective-permute-start.59) | collective-permute-done | bytes 16416 | tf_op jit(solution)/shard_map/ppermute | solution.py:33
  134.8 1.0 shard_map.125
  (164 shorter events, 19.4 us)
Async XLA Ops:
  0.6 26.5 %copy-start.2 = (f32[1,4,256,128]{3,2,1,0:T(8,128)S(1)}, f32[1,4,256,128]{3,2,1,0:T(8,128)}, u32[]{:S(2)}) copy-start(f32[1,4,256,128]{3,2,1,0:T(8,128)} %rhs_ref.3) | copy-start | bytes 1572868
  2.4 20.4 %copy-start.4 = (f32[64,256]{1,0:T(8,128)S(1)}, f32[64,256]{1,0:T(8,128)}, u32[]{:S(2)}) copy-start(f32[64,256]{1,0:T(8,128)} %get-tuple-element.54.refs_0_) | copy-start | bytes 196612
  2.4 10.1 %collective-permute-start = (f32[64,256]{1,0:T(8,128)}, f32[64,256]{1,0:T(8,128)S(1)}, u32[]{:S(2)}, u32[]{:S(2)}) collective-permute-start(f32[64,256]{1,0:T(8,128)} %get-tuple-element.53.refs_0_), channel_id=1, source_target_pairs={{0,1},{1,0},{2,3},{3,2},{4,5},{5,4},{6,7},{7,6},{8,9},{9,8},{10,11... | collective-permute-start | bytes 196616 | tf_op jit(solution)/shard_map/ppermute | solution.py:33
  5.5 9.2 %collective-permute-start.1 = (f32[64,256]{1,0:T(8,128)}, f32[64,256]{1,0:T(8,128)S(1)}, u32[]{:S(2)}, u32[]{:S(2)}) collective-permute-start(f32[64,256]{1,0:T(8,128)} %get-tuple-element.53.refs_0_), channel_id=1, source_target_pairs={{0,2},{1,3},{2,0},{3,1},{4,6},{5,7},{6,4},{7,5},{8,10},{9,11},{10,... | collective-permute-start | bytes 196616 | tf_op jit(solution)/shard_map/ppermute | solution.py:33
  8.0 6.8 %collective-permute-start.2 = (f32[64,256]{1,0:T(8,128)}, f32[64,256]{1,0:T(8,128)S(1)}, u32[]{:S(2)}, u32[]{:S(2)}) collective-permute-start(f32[64,256]{1,0:T(8,128)} %get-tuple-element.53.refs_0_), channel_id=1, source_target_pairs={{0,3},{1,2},{2,1},{3,0},{4,7},{5,6},{6,5},{7,4},{8,11},{9,10},{10,... | collective-permute-start | bytes 196616 | tf_op jit(solution)/shard_map/ppermute | solution.py:33
  8.0 13.3 %collective-permute-start.3 = (f32[64,256]{1,0:T(8,128)}, f32[64,256]{1,0:T(8,128)S(1)}, u32[]{:S(2)}, u32[]{:S(2)}) collective-permute-start(f32[64,256]{1,0:T(8,128)} %get-tuple-element.54.refs_0_), channel_id=1, source_target_pairs={{0,1},{1,0},{2,3},{3,2},{4,5},{5,4},{6,7},{7,6},{8,9},{9,8},{10,11... | collective-permute-start | bytes 196616 | tf_op jit(solution)/shard_map/ppermute | solution.py:33
  8.9 13.8 %collective-permute-start.4 = (f32[64,256]{1,0:T(8,128)}, f32[64,256]{1,0:T(8,128)S(1)}, u32[]{:S(2)}, u32[]{:S(2)}) collective-permute-start(f32[64,256]{1,0:T(8,128)} %get-tuple-element.54.refs_0_), channel_id=1, source_target_pairs={{0,2},{1,3},{2,0},{3,1},{4,6},{5,7},{6,4},{7,5},{8,10},{9,11},{10,... | collective-permute-start | bytes 196616 | tf_op jit(solution)/shard_map/ppermute | solution.py:33
  12.4 10.3 %collective-permute-start.5 = (f32[64,256]{1,0:T(8,128)}, f32[64,256]{1,0:T(8,128)S(1)}, u32[]{:S(2)}, u32[]{:S(2)}) collective-permute-start(f32[64,256]{1,0:T(8,128)} %get-tuple-element.54.refs_0_), channel_id=1, source_target_pairs={{0,3},{1,2},{2,1},{3,0},{4,7},{5,6},{6,5},{7,4},{8,11},{9,10},{10,... | collective-permute-start | bytes 196616 | tf_op jit(solution)/shard_map/ppermute | solution.py:33
  16.1 11.0 %collective-permute-start.6 = (f32[64,256]{1,0:T(8,128)S(1)}, f32[64,256]{1,0:T(8,128)S(1)}, u32[]{:S(2)}, u32[]{:S(2)}) collective-permute-start(f32[64,256]{1,0:T(8,128)S(1)} %shard_map.114.refs_0_), channel_id=1, source_target_pairs={{0,1},{1,0},{2,3},{3,2},{4,5},{5,4},{6,7},{7,6},{8,9},{9,8},{10,11... | collective-permute-start | bytes 196616 | tf_op jit(solution)/shard_map/ppermute | solution.py:33
  19.4 7.3 %collective-permute-start.7 = (f32[64,256]{1,0:T(8,128)S(1)}, f32[64,256]{1,0:T(8,128)S(1)}, u32[]{:S(2)}, u32[]{:S(2)}) collective-permute-start(f32[64,256]{1,0:T(8,128)S(1)} %shard_map.114.refs_0_), channel_id=1, source_target_pairs={{0,2},{1,3},{2,0},{3,1},{4,6},{5,7},{6,4},{7,5},{8,10},{9,11},{10,... | collective-permute-start | bytes 196616 | tf_op jit(solution)/shard_map/ppermute | solution.py:33
  21.3 6.5 %collective-permute-start.8 = (f32[64,256]{1,0:T(8,128)S(1)}, f32[64,256]{1,0:T(8,128)S(1)}, u32[]{:S(2)}, u32[]{:S(2)}) collective-permute-start(f32[64,256]{1,0:T(8,128)S(1)} %shard_map.114.refs_0_), channel_id=1, source_target_pairs={{0,3},{1,2},{2,1},{3,0},{4,7},{5,6},{6,5},{7,4},{8,11},{9,10},{10,... | collective-permute-start | bytes 196616 | tf_op jit(solution)/shard_map/ppermute | solution.py:33
  23.2 11.8 %collective-permute-start.9 = (f32[64,256]{1,0:T(8,128)S(1)}, f32[64,256]{1,0:T(8,128)S(1)}, u32[]{:S(2)}, u32[]{:S(2)}) collective-permute-start(f32[64,256]{1,0:T(8,128)S(1)} %shard_map.115.refs_1_), channel_id=1, source_target_pairs={{0,2},{1,3},{2,0},{3,1},{4,6},{5,7},{6,4},{7,5},{8,10},{9,11},{10,... | collective-permute-start | bytes 196616 | tf_op jit(solution)/shard_map/ppermute | solution.py:33
  25.3 10.2 %collective-permute-start.13 = (f32[64,256]{1,0:T(8,128)S(1)}, f32[64,256]{1,0:T(8,128)S(1)}, u32[]{:S(2)}, u32[]{:S(2)}) collective-permute-start(f32[64,256]{1,0:T(8,128)S(1)} %shard_map.115.refs_1_), channel_id=1, source_target_pairs={{0,3},{1,2},{2,1},{3,0},{4,7},{5,6},{6,5},{7,4},{8,11},{9,10},{10,... | collective-permute-start | bytes 196616 | tf_op jit(solution)/shard_map/ppermute | solution.py:33
  26.8 8.7 %collective-permute-start.12 = (f32[64,256]{1,0:T(8,128)S(1)}, f32[64,256]{1,0:T(8,128)S(1)}, u32[]{:S(2)}, u32[]{:S(2)}) collective-permute-start(f32[64,256]{1,0:T(8,128)S(1)} %shard_map.115.refs_1_), channel_id=1, source_target_pairs={{0,1},{1,0},{2,3},{3,2},{4,5},{5,4},{6,7},{7,6},{8,9},{9,8},{10,11... | collective-permute-start | bytes 196616 | tf_op jit(solution)/shard_map/ppermute | solution.py:33
  28.5 11.7 %collective-permute-start.11 = (f32[64,256]{1,0:T(8,128)S(1)}, f32[64,256]{1,0:T(8,128)S(1)}, u32[]{:S(2)}, u32[]{:S(2)}) collective-permute-start(f32[64,256]{1,0:T(8,128)S(1)} %get-tuple-element.57), channel_id=1, source_target_pairs={{0,2},{1,3},{2,0},{3,1},{4,6},{5,7},{6,4},{7,5},{8,10},{9,11},{10,... | collective-permute-start | bytes 196616 | tf_op jit(solution)/shard_map/ppermute | solution.py:33
  34.8 6.2 %collective-permute-start.14 = (f32[64,256]{1,0:T(8,128)S(1)}, f32[64,256]{1,0:T(8,128)S(1)}, u32[]{:S(2)}, u32[]{:S(2)}) collective-permute-start(f32[64,256]{1,0:T(8,128)S(1)} %get-tuple-element.57), channel_id=1, source_target_pairs={{0,3},{1,2},{2,1},{3,0},{4,7},{5,6},{6,5},{7,4},{8,11},{9,10},{10,... | collective-permute-start | bytes 196616 | tf_op jit(solution)/shard_map/ppermute | solution.py:33
  35.0 5.6 %collective-permute-start.10 = (f32[64,256]{1,0:T(8,128)S(1)}, f32[64,256]{1,0:T(8,128)S(1)}, u32[]{:S(2)}, u32[]{:S(2)}) collective-permute-start(f32[64,256]{1,0:T(8,128)S(1)} %get-tuple-element.57), channel_id=1, source_target_pairs={{0,1},{1,0},{2,3},{3,2},{4,5},{5,4},{6,7},{7,6},{8,9},{9,8},{10,11... | collective-permute-start | bytes 196616 | tf_op jit(solution)/shard_map/ppermute | solution.py:33
  36.1 9.2 %collective-permute-start.16 = (f32[64,256]{1,0:T(8,128)S(1)}, f32[64,256]{1,0:T(8,128)S(1)}, u32[]{:S(2)}, u32[]{:S(2)}) collective-permute-start(f32[64,256]{1,0:T(8,128)S(1)} %get-tuple-element.60), channel_id=1, source_target_pairs={{0,2},{1,3},{2,0},{3,1},{4,6},{5,7},{6,4},{7,5},{8,10},{9,11},{10,... | collective-permute-start | bytes 196616 | tf_op jit(solution)/shard_map/ppermute | solution.py:33
  40.0 7.4 %collective-permute-start.17 = (f32[64,256]{1,0:T(8,128)S(1)}, f32[64,256]{1,0:T(8,128)S(1)}, u32[]{:S(2)}, u32[]{:S(2)}) collective-permute-start(f32[64,256]{1,0:T(8,128)S(1)} %get-tuple-element.60), channel_id=1, source_target_pairs={{0,3},{1,2},{2,1},{3,0},{4,7},{5,6},{6,5},{7,4},{8,11},{9,10},{10,... | collective-permute-start | bytes 196616 | tf_op jit(solution)/shard_map/ppermute | solution.py:33
  40.2 7.1 %collective-permute-start.15 = (f32[64,256]{1,0:T(8,128)S(1)}, f32[64,256]{1,0:T(8,128)S(1)}, u32[]{:S(2)}, u32[]{:S(2)}) collective-permute-start(f32[64,256]{1,0:T(8,128)S(1)} %get-tuple-element.60), channel_id=1, source_target_pairs={{0,1},{1,0},{2,3},{3,2},{4,5},{5,4},{6,7},{7,6},{8,9},{9,8},{10,11... | collective-permute-start | bytes 196616 | tf_op jit(solution)/shard_map/ppermute | solution.py:33
  41.7 10.0 %collective-permute-start.19 = (f32[64,256]{1,0:T(8,128)S(1)}, f32[64,256]{1,0:T(8,128)S(1)}, u32[]{:S(2)}, u32[]{:S(2)}) collective-permute-start(f32[64,256]{1,0:T(8,128)S(1)} %get-tuple-element.62.refs_2_), channel_id=1, source_target_pairs={{0,2},{1,3},{2,0},{3,1},{4,6},{5,7},{6,4},{7,5},{8,10},{9,11},{10,... | collective-permute-start | bytes 196616 | tf_op jit(solution)/shard_map/ppermute | solution.py:33
  45.1 6.7 %collective-permute-start.20 = (f32[64,256]{1,0:T(8,128)S(1)}, f32[64,256]{1,0:T(8,128)S(1)}, u32[]{:S(2)}, u32[]{:S(2)}) collective-permute-start(f32[64,256]{1,0:T(8,128)S(1)} %get-tuple-element.62.refs_2_), channel_id=1, source_target_pairs={{0,3},{1,2},{2,1},{3,0},{4,7},{5,6},{6,5},{7,4},{8,11},{9,10},{10,... | collective-permute-start | bytes 196616 | tf_op jit(solution)/shard_map/ppermute | solution.py:33
  45.4 6.4 %collective-permute-start.18 = (f32[64,256]{1,0:T(8,128)S(1)}, f32[64,256]{1,0:T(8,128)S(1)}, u32[]{:S(2)}, u32[]{:S(2)}) collective-permute-start(f32[64,256]{1,0:T(8,128)S(1)} %get-tuple-element.62.refs_2_), channel_id=1, source_target_pairs={{0,1},{1,0},{2,3},{3,2},{4,5},{5,4},{6,7},{7,6},{8,9},{9,8},{10,11... | collective-permute-start | bytes 196616 | tf_op jit(solution)/shard_map/ppermute | solution.py:33
  48.0 9.4 %collective-permute-start.21 = (f32[64,256]{1,0:T(8,128)S(1)}, f32[64,256]{1,0:T(8,128)S(1)}, u32[]{:S(2)}, u32[]{:S(2)}) collective-permute-start(f32[64,256]{1,0:T(8,128)S(1)} %get-tuple-element.66.refs_3_), channel_id=1, source_target_pairs={{0,2},{1,3},{2,0},{3,1},{4,6},{5,7},{6,4},{7,5},{8,10},{9,11},{10,... | collective-permute-start | bytes 196616 | tf_op jit(solution)/shard_map/ppermute | solution.py:33
  50.3 8.6 %collective-permute-start.25 = (f32[64,256]{1,0:T(8,128)S(1)}, f32[64,256]{1,0:T(8,128)S(1)}, u32[]{:S(2)}, u32[]{:S(2)}) collective-permute-start(f32[64,256]{1,0:T(8,128)S(1)} %get-tuple-element.66.refs_3_), channel_id=1, source_target_pairs={{0,3},{1,2},{2,1},{3,0},{4,7},{5,6},{6,5},{7,4},{8,11},{9,10},{10,... | collective-permute-start | bytes 196616 | tf_op jit(solution)/shard_map/ppermute | solution.py:33
  51.7 7.2 %collective-permute-start.24 = (f32[64,256]{1,0:T(8,128)S(1)}, f32[64,256]{1,0:T(8,128)S(1)}, u32[]{:S(2)}, u32[]{:S(2)}) collective-permute-start(f32[64,256]{1,0:T(8,128)S(1)} %get-tuple-element.66.refs_3_), channel_id=1, source_target_pairs={{0,1},{1,0},{2,3},{3,2},{4,5},{5,4},{6,7},{7,6},{8,9},{9,8},{10,11... | collective-permute-start | bytes 196616 | tf_op jit(solution)/shard_map/ppermute | solution.py:33
  52.5 11.7 %collective-permute-start.23 = (f32[64,256]{1,0:T(8,128)S(1)}, f32[64,256]{1,0:T(8,128)S(1)}, u32[]{:S(2)}, u32[]{:S(2)}) collective-permute-start(f32[64,256]{1,0:T(8,128)S(1)} %get-tuple-element.65), channel_id=1, source_target_pairs={{0,2},{1,3},{2,0},{3,1},{4,6},{5,7},{6,4},{7,5},{8,10},{9,11},{10,... | collective-permute-start | bytes 196616 | tf_op jit(solution)/shard_map/ppermute | solution.py:33
  55.5 9.6 %collective-permute-start.26 = (f32[64,256]{1,0:T(8,128)S(1)}, f32[64,256]{1,0:T(8,128)S(1)}, u32[]{:S(2)}, u32[]{:S(2)}) collective-permute-start(f32[64,256]{1,0:T(8,128)S(1)} %get-tuple-element.65), channel_id=1, source_target_pairs={{0,3},{1,2},{2,1},{3,0},{4,7},{5,6},{6,5},{7,4},{8,11},{9,10},{10,... | collective-permute-start | bytes 196616 | tf_op jit(solution)/shard_map/ppermute | solution.py:33
  57.4 7.6 %collective-permute-start.22 = (f32[64,256]{1,0:T(8,128)S(1)}, f32[64,256]{1,0:T(8,128)S(1)}, u32[]{:S(2)}, u32[]{:S(2)}) collective-permute-start(f32[64,256]{1,0:T(8,128)S(1)} %get-tuple-element.65), channel_id=1, source_target_pairs={{0,1},{1,0},{2,3},{3,2},{4,5},{5,4},{6,7},{7,6},{8,9},{9,8},{10,11... | collective-permute-start | bytes 196616 | tf_op jit(solution)/shard_map/ppermute | solution.py:33
  59.7 9.8 %collective-permute-start.28 = (f32[64,256]{1,0:T(8,128)S(1)}, f32[64,256]{1,0:T(8,128)S(1)}, u32[]{:S(2)}, u32[]{:S(2)}) collective-permute-start(f32[64,256]{1,0:T(8,128)S(1)} %get-tuple-element.68), channel_id=1, source_target_pairs={{0,2},{1,3},{2,0},{3,1},{4,6},{5,7},{6,4},{7,5},{8,10},{9,11},{10,... | collective-permute-start | bytes 196616 | tf_op jit(solution)/shard_map/ppermute | solution.py:33
  61.9 9.1 %collective-permute-start.29 = (f32[64,256]{1,0:T(8,128)S(1)}, f32[64,256]{1,0:T(8,128)S(1)}, u32[]{:S(2)}, u32[]{:S(2)}) collective-permute-start(f32[64,256]{1,0:T(8,128)S(1)} %get-tuple-element.68), channel_id=1, source_target_pairs={{0,3},{1,2},{2,1},{3,0},{4,7},{5,6},{6,5},{7,4},{8,11},{9,10},{10,... | collective-permute-start | bytes 196616 | tf_op jit(solution)/shard_map/ppermute | solution.py:33
  64.2 6.7 %collective-permute-start.27 = (f32[64,256]{1,0:T(8,128)S(1)}, f32[64,256]{1,0:T(8,128)S(1)}, u32[]{:S(2)}, u32[]{:S(2)}) collective-permute-start(f32[64,256]{1,0:T(8,128)S(1)} %get-tuple-element.68), channel_id=1, source_target_pairs={{0,1},{1,0},{2,3},{3,2},{4,5},{5,4},{6,7},{7,6},{8,9},{9,8},{10,11... | collective-permute-start | bytes 196616 | tf_op jit(solution)/shard_map/ppermute | solution.py:33
  65.8 8.9 %collective-permute-start.31 = (f32[64,256]{1,0:T(8,128)S(1)}, f32[64,256]{1,0:T(8,128)S(1)}, u32[]{:S(2)}, u32[]{:S(2)}) collective-permute-start(f32[64,256]{1,0:T(8,128)S(1)} %get-tuple-element.70.refs_4_), channel_id=1, source_target_pairs={{0,2},{1,3},{2,0},{3,1},{4,6},{5,7},{6,4},{7,5},{8,10},{9,11},{10,... | collective-permute-start | bytes 196616 | tf_op jit(solution)/shard_map/ppermute | solution.py:33
  67.1 9.1 %collective-permute-start.32 = (f32[64,256]{1,0:T(8,128)S(1)}, f32[64,256]{1,0:T(8,128)S(1)}, u32[]{:S(2)}, u32[]{:S(2)}) collective-permute-start(f32[64,256]{1,0:T(8,128)S(1)} %get-tuple-element.70.refs_4_), channel_id=1, source_target_pairs={{0,3},{1,2},{2,1},{3,0},{4,7},{5,6},{6,5},{7,4},{8,11},{9,10},{10,... | collective-permute-start | bytes 196616 | tf_op jit(solution)/shard_map/ppermute | solution.py:33
  69.4 6.8 %collective-permute-start.30 = (f32[64,256]{1,0:T(8,128)S(1)}, f32[64,256]{1,0:T(8,128)S(1)}, u32[]{:S(2)}, u32[]{:S(2)}) collective-permute-start(f32[64,256]{1,0:T(8,128)S(1)} %get-tuple-element.70.refs_4_), channel_id=1, source_target_pairs={{0,1},{1,0},{2,3},{3,2},{4,5},{5,4},{6,7},{7,6},{8,9},{9,8},{10,11... | collective-permute-start | bytes 196616 | tf_op jit(solution)/shard_map/ppermute | solution.py:33
  71.7 8.2 %collective-permute-start.33 = (f32[64,256]{1,0:T(8,128)S(1)}, f32[64,256]{1,0:T(8,128)S(1)}, u32[]{:S(2)}, u32[]{:S(2)}) collective-permute-start(f32[64,256]{1,0:T(8,128)S(1)} %get-tuple-element.74.refs_5_), channel_id=1, source_target_pairs={{0,2},{1,3},{2,0},{3,1},{4,6},{5,7},{6,4},{7,5},{8,10},{9,11},{10,... | collective-permute-start | bytes 196616 | tf_op jit(solution)/shard_map/ppermute | solution.py:33
  73.2 8.6 %collective-permute-start.37 = (f32[64,256]{1,0:T(8,128)S(1)}, f32[64,256]{1,0:T(8,128)S(1)}, u32[]{:S(2)}, u32[]{:S(2)}) collective-permute-start(f32[64,256]{1,0:T(8,128)S(1)} %get-tuple-element.74.refs_5_), channel_id=1, source_target_pairs={{0,3},{1,2},{2,1},{3,0},{4,7},{5,6},{6,5},{7,4},{8,11},{9,10},{10,... | collective-permute-start | bytes 196616 | tf_op jit(solution)/shard_map/ppermute | solution.py:33
  74.7 7.2 %collective-permute-start.36 = (f32[64,256]{1,0:T(8,128)S(1)}, f32[64,256]{1,0:T(8,128)S(1)}, u32[]{:S(2)}, u32[]{:S(2)}) collective-permute-start(f32[64,256]{1,0:T(8,128)S(1)} %get-tuple-element.74.refs_5_), channel_id=1, source_target_pairs={{0,1},{1,0},{2,3},{3,2},{4,5},{5,4},{6,7},{7,6},{8,9},{9,8},{10,11... | collective-permute-start | bytes 196616 | tf_op jit(solution)/shard_map/ppermute | solution.py:33
  76.9 10.1 %collective-permute-start.35 = (f32[64,256]{1,0:T(8,128)S(1)}, f32[64,256]{1,0:T(8,128)S(1)}, u32[]{:S(2)}, u32[]{:S(2)}) collective-permute-start(f32[64,256]{1,0:T(8,128)S(1)} %get-tuple-element.73), channel_id=1, source_target_pairs={{0,2},{1,3},{2,0},{3,1},{4,6},{5,7},{6,4},{7,5},{8,10},{9,11},{10,... | collective-permute-start | bytes 196616 | tf_op jit(solution)/shard_map/ppermute | solution.py:33
  78.4 9.1 %collective-permute-start.38 = (f32[64,256]{1,0:T(8,128)S(1)}, f32[64,256]{1,0:T(8,128)S(1)}, u32[]{:S(2)}, u32[]{:S(2)}) collective-permute-start(f32[64,256]{1,0:T(8,128)S(1)} %get-tuple-element.73), channel_id=1, source_target_pairs={{0,3},{1,2},{2,1},{3,0},{4,7},{5,6},{6,5},{7,4},{8,11},{9,10},{10,... | collective-permute-start | bytes 196616 | tf_op jit(solution)/shard_map/ppermute | solution.py:33
  79.9 7.6 %collective-permute-start.34 = (f32[64,256]{1,0:T(8,128)S(1)}, f32[64,256]{1,0:T(8,128)S(1)}, u32[]{:S(2)}, u32[]{:S(2)}) collective-permute-start(f32[64,256]{1,0:T(8,128)S(1)} %get-tuple-element.73), channel_id=1, source_target_pairs={{0,1},{1,0},{2,3},{3,2},{4,5},{5,4},{6,7},{7,6},{8,9},{9,8},{10,11... | collective-permute-start | bytes 196616 | tf_op jit(solution)/shard_map/ppermute | solution.py:33
  81.9 18.4 %copy-start = (f32[1,1,3,128,1024]{4,3,2,1,0:T(8,128)S(1)}, f32[1,1,3,128,1024]{4,3,2,1,0:T(8,128)}, u32[]{:S(2)}) copy-start(f32[1,1,3,128,1024]{4,3,2,1,0:T(8,128)} %param.13) | copy-start | bytes 4718596
  82.6 9.6 %collective-permute-start.40 = (f32[64,256]{1,0:T(8,128)S(1)}, f32[64,256]{1,0:T(8,128)S(1)}, u32[]{:S(2)}, u32[]{:S(2)}) collective-permute-start(f32[64,256]{1,0:T(8,128)S(1)} %get-tuple-element.76), channel_id=1, source_target_pairs={{0,2},{1,3},{2,0},{3,1},{4,6},{5,7},{6,4},{7,5},{8,10},{9,11},{10,... | collective-permute-start | bytes 196616 | tf_op jit(solution)/shard_map/ppermute | solution.py:33
  84.5 9.3 %collective-permute-start.41 = (f32[64,256]{1,0:T(8,128)S(1)}, f32[64,256]{1,0:T(8,128)S(1)}, u32[]{:S(2)}, u32[]{:S(2)}) collective-permute-start(f32[64,256]{1,0:T(8,128)S(1)} %get-tuple-element.76), channel_id=1, source_target_pairs={{0,3},{1,2},{2,1},{3,0},{4,7},{5,6},{6,5},{7,4},{8,11},{9,10},{10,... | collective-permute-start | bytes 196616 | tf_op jit(solution)/shard_map/ppermute | solution.py:33
  87.0 6.7 %collective-permute-start.39 = (f32[64,256]{1,0:T(8,128)S(1)}, f32[64,256]{1,0:T(8,128)S(1)}, u32[]{:S(2)}, u32[]{:S(2)}) collective-permute-start(f32[64,256]{1,0:T(8,128)S(1)} %get-tuple-element.76), channel_id=1, source_target_pairs={{0,1},{1,0},{2,3},{3,2},{4,5},{5,4},{6,7},{7,6},{8,9},{9,8},{10,11... | collective-permute-start | bytes 196616 | tf_op jit(solution)/shard_map/ppermute | solution.py:33
  88.2 9.1 %collective-permute-start.43 = (f32[64,256]{1,0:T(8,128)S(1)}, f32[64,256]{1,0:T(8,128)S(1)}, u32[]{:S(2)}, u32[]{:S(2)}) collective-permute-start(f32[64,256]{1,0:T(8,128)S(1)} %get-tuple-element.78.refs_6_), channel_id=1, source_target_pairs={{0,2},{1,3},{2,0},{3,1},{4,6},{5,7},{6,4},{7,5},{8,10},{9,11},{10,... | collective-permute-start | bytes 196616 | tf_op jit(solution)/shard_map/ppermute | solution.py:33
  89.7 8.4 %collective-permute-start.44 = (f32[64,256]{1,0:T(8,128)S(1)}, f32[64,256]{1,0:T(8,128)S(1)}, u32[]{:S(2)}, u32[]{:S(2)}) collective-permute-start(f32[64,256]{1,0:T(8,128)S(1)} %get-tuple-element.78.refs_6_), channel_id=1, source_target_pairs={{0,3},{1,2},{2,1},{3,0},{4,7},{5,6},{6,5},{7,4},{8,11},{9,10},{10,... | collective-permute-start | bytes 196616 | tf_op jit(solution)/shard_map/ppermute | solution.py:33
  92.2 5.8 %collective-permute-start.42 = (f32[64,256]{1,0:T(8,128)S(1)}, f32[64,256]{1,0:T(8,128)S(1)}, u32[]{:S(2)}, u32[]{:S(2)}) collective-permute-start(f32[64,256]{1,0:T(8,128)S(1)} %get-tuple-element.78.refs_6_), channel_id=1, source_target_pairs={{0,1},{1,0},{2,3},{3,2},{4,5},{5,4},{6,7},{7,6},{8,9},{9,8},{10,11... | collective-permute-start | bytes 196616 | tf_op jit(solution)/shard_map/ppermute | solution.py:33
  94.5 5.8 %collective-permute-start.46 = (f32[64,256]{1,0:T(8,128)S(1)}, f32[64,256]{1,0:T(8,128)S(1)}, u32[]{:S(2)}, u32[]{:S(2)}) collective-permute-start(f32[64,256]{1,0:T(8,128)S(1)} %get-tuple-element.80.refs_7_), channel_id=1, source_target_pairs={{0,2},{1,3},{2,0},{3,1},{4,6},{5,7},{6,4},{7,5},{8,10},{9,11},{10,... | collective-permute-start | bytes 196616 | tf_op jit(solution)/shard_map/ppermute | solution.py:33
  95.0 6.9 %collective-permute-start.47 = (f32[64,256]{1,0:T(8,128)S(1)}, f32[64,256]{1,0:T(8,128)S(1)}, u32[]{:S(2)}, u32[]{:S(2)}) collective-permute-start(f32[64,256]{1,0:T(8,128)S(1)} %get-tuple-element.80.refs_7_), channel_id=1, source_target_pairs={{0,3},{1,2},{2,1},{3,0},{4,7},{5,6},{6,5},{7,4},{8,11},{9,10},{10,... | collective-permute-start | bytes 196616 | tf_op jit(solution)/shard_map/ppermute | solution.py:33
  97.4 4.5 %collective-permute-start.45 = (f32[64,256]{1,0:T(8,128)S(1)}, f32[64,256]{1,0:T(8,128)S(1)}, u32[]{:S(2)}, u32[]{:S(2)}) collective-permute-start(f32[64,256]{1,0:T(8,128)S(1)} %get-tuple-element.80.refs_7_), channel_id=1, source_target_pairs={{0,1},{1,0},{2,3},{3,2},{4,5},{5,4},{6,7},{7,6},{8,9},{9,8},{10,11... | collective-permute-start | bytes 196616 | tf_op jit(solution)/shard_map/ppermute | solution.py:33
  103.2 1.4 %collective-permute-start.48 = (f32[4,16,512]{2,1,0:T(8,128)S(1)}, f32[4,16,512]{2,1,0:T(8,128)S(1)}, u32[]{:S(2)}, u32[]{:S(2)}) collective-permute-start(f32[4,16,512]{2,1,0:T(8,128)S(1)} %get-tuple-element.84), channel_id=1, source_target_pairs={{0,4},{4,0},{8,12},{12,8},{16,20},{20,16},{24,28},{28,24},{1,5},{5... | collective-permute-start | bytes 393224 | tf_op jit(solution)/shard_map/ppermute | solution.py:282
  104.6 5.5 %collective-permute-start.49 = (f32[2,16,512]{2,1,0:T(8,128)S(1)}, f32[2,16,512]{2,1,0:T(8,128)S(1)}, u32[]{:S(2)}, u32[]{:S(2)}) collective-permute-start(f32[2,16,512]{2,1,0:T(8,128)S(1)} %get-tuple-element.86), channel_id=1, source_target_pairs={{0,24},{4,28},{8,16},{12,20},{16,8},{20,12},{24,0},{28,4},{1,25},{... | collective-permute-start | bytes 196616 | tf_op jit(solution)/shard_map/ppermute | solution.py:81
  107.7 4.3 %collective-permute-start.50 = (f32[2,16,512]{2,1,0:T(8,128)S(1)}, f32[2,16,512]{2,1,0:T(8,128)S(1)}, u32[]{:S(2)}, u32[]{:S(2)}) collective-permute-start(f32[2,16,512]{2,1,0:T(8,128)S(1)} %get-tuple-element.87), channel_id=1, source_target_pairs={{0,16},{4,20},{8,24},{12,28},{16,0},{20,4},{24,8},{28,12},{1,17},{... | collective-permute-start | bytes 196616 | tf_op jit(solution)/shard_map/ppermute | solution.py:81
  107.7 4.3 %collective-permute-start.51 = (f32[2,16,512]{2,1,0:T(8,128)S(1)}, f32[2,16,512]{2,1,0:T(8,128)S(1)}, u32[]{:S(2)}, u32[]{:S(2)}) collective-permute-start(f32[2,16,512]{2,1,0:T(8,128)S(1)} %get-tuple-element.88), channel_id=1, source_target_pairs={{0,8},{4,12},{8,0},{12,4},{16,24},{20,28},{24,16},{28,20},{1,9},{5... | collective-permute-start | bytes 196616 | tf_op jit(solution)/shard_map/ppermute | solution.py:81
  112.4 6.1 %collective-permute-start.52 = (f32[16,1024]{1,0:T(8,128)S(1)}, f32[16,1024]{1,0:T(8,128)S(1)}, u32[]{:S(2)}, u32[]{:S(2)}) collective-permute-start(f32[16,1024]{1,0:T(8,128)S(1)} %get-tuple-element.90.refs_2_.refs_0_), channel_id=1, source_target_pairs={{0,2},{1,3},{2,0},{3,1},{4,6},{5,7},{6,4},{7,5},{8,10},{9,11},{10,... | collective-permute-start | bytes 196616 | tf_op jit(solution)/shard_map/ppermute | solution.py:33
  113.4 6.2 %collective-permute-start.53 = (f32[16,1024]{1,0:T(8,128)S(1)}, f32[16,1024]{1,0:T(8,128)S(1)}, u32[]{:S(2)}, u32[]{:S(2)}) collective-permute-start(f32[16,1024]{1,0:T(8,128)S(1)} %get-tuple-element.90.refs_2_.refs_0_), channel_id=1, source_target_pairs={{0,3},{1,2},{2,1},{3,0},{4,7},{5,6},{6,5},{7,4},{8,11},{9,10},{10,... | collective-permute-start | bytes 196616 | tf_op jit(solution)/shard_map/ppermute | solution.py:33
  114.8 5.1 %collective-permute-start.54 = (f32[16,1024]{1,0:T(8,128)S(1)}, f32[16,1024]{1,0:T(8,128)S(1)}, u32[]{:S(2)}, u32[]{:S(2)}) collective-permute-start(f32[16,1024]{1,0:T(8,128)S(1)} %get-tuple-element.90.refs_2_.refs_0_), channel_id=1, source_target_pairs={{0,1},{1,0},{2,3},{3,2},{4,5},{5,4},{6,7},{7,6},{8,9},{9,8},{10,11... | collective-permute-start | bytes 196616 | tf_op jit(solution)/shard_map/ppermute | solution.py:33
  120.3 5.2 %collective-permute-start.55 = (f32[16,512]{1,0:T(8,128)S(1)}, f32[16,512]{1,0:T(8,128)S(1)}, u32[]{:S(2)}, u32[]{:S(2)}) collective-permute-start(f32[16,512]{1,0:T(8,128)S(1)} %get-tuple-element.98), channel_id=1, source_target_pairs={{0,2},{1,3},{2,0},{3,1},{4,6},{5,7},{6,4},{7,5},{8,10},{9,11},{10,... | collective-permute-start | bytes 98312 | tf_op jit(solution)/shard_map/ppermute | solution.py:33
  121.4 5.7 %collective-permute-start.56 = (f32[16,512]{1,0:T(8,128)S(1)}, f32[16,512]{1,0:T(8,128)S(1)}, u32[]{:S(2)}, u32[]{:S(2)}) collective-permute-start(f32[16,512]{1,0:T(8,128)S(1)} %get-tuple-element.99), channel_id=1, source_target_pairs={{0,3},{1,2},{2,1},{3,0},{4,7},{5,6},{6,5},{7,4},{8,11},{9,10},{10,... | collective-permute-start | bytes 98312 | tf_op jit(solution)/shard_map/ppermute | solution.py:33
  123.2 4.2 %collective-permute-start.57 = (f32[16,512]{1,0:T(8,128)S(1)}, f32[16,512]{1,0:T(8,128)S(1)}, u32[]{:S(2)}, u32[]{:S(2)}) collective-permute-start(f32[16,512]{1,0:T(8,128)S(1)} %get-tuple-element.100), channel_id=1, source_target_pairs={{0,1},{1,0},{2,3},{3,2},{4,5},{5,4},{6,7},{7,6},{8,9},{9,8},{10,11... | collective-permute-start | bytes 98312 | tf_op jit(solution)/shard_map/ppermute | solution.py:33
  128.3 4.6 %collective-permute-start.58 = (f32[16,256]{1,0:T(8,128)S(1)}, f32[16,256]{1,0:T(8,128)S(1)}, u32[]{:S(2)}, u32[]{:S(2)}) collective-permute-start(f32[16,256]{1,0:T(8,128)S(1)} %get-tuple-element.103.refs_0_), channel_id=1, source_target_pairs={{0,2},{1,3},{2,0},{3,1},{4,6},{5,7},{6,4},{7,5},{8,10},{9,11},{10,... | collective-permute-start | bytes 49160 | tf_op jit(solution)/shard_map/ppermute | solution.py:33
  129.1 5.5 %collective-permute-start.59 = (f32[16,256]{1,0:T(8,128)S(1)}, f32[16,256]{1,0:T(8,128)S(1)}, u32[]{:S(2)}, u32[]{:S(2)}) collective-permute-start(f32[16,256]{1,0:T(8,128)S(1)} %get-tuple-element.103.refs_0_), channel_id=1, source_target_pairs={{0,3},{1,2},{2,1},{3,0},{4,7},{5,6},{6,5},{7,4},{8,11},{9,10},{10,... | collective-permute-start | bytes 49160 | tf_op jit(solution)/shard_map/ppermute | solution.py:33
  131.0 3.9 %collective-permute-start.60 = (f32[16,256]{1,0:T(8,128)S(1)}, f32[16,256]{1,0:T(8,128)S(1)}, u32[]{:S(2)}, u32[]{:S(2)}) collective-permute-start(f32[16,256]{1,0:T(8,128)S(1)} %get-tuple-element.103.refs_0_), channel_id=1, source_target_pairs={{0,1},{1,0},{2,3},{3,2},{4,5},{5,4},{6,7},{7,6},{8,9},{9,8},{10,11... | collective-permute-start | bytes 49160 | tf_op jit(solution)/shard_map/ppermute | solution.py:33
  (8 other events, 103.0 us)

commit v22 on v21

--- a/solution.py
+++ b/solution.py
@@ -247,7 +247,6 @@
         [rhs],
         [ANY],
         scratch=[pltpu.VMEM((rows, count), jnp.float32), pltpu.SemaphoreType.DMA(())],
-        limit=121 * 2**19,
     )
 
 
@@ -397,18 +396,20 @@
     def body(*refs):
         own_ref, other_ref = refs[:2]
         held = refs[2 : members + 1]
-        top_ref, rest_ref, out, left, whole = refs[members + 1 :]
+        top_ref, rest_ref, out = refs[members + 1 : members + 4]
+        whole = refs[-1]
         total = other_ref[...]
         for ref in held:
             total = total + ref[:, rows:]
-        left[...] = total
+        if width > rows:
+            refs[members + 4][...] = total
         pieces = [ref[:, :rows] for ref in held[-1:] + held[:-1]]
         put_in_order([own_ref[...]] + pieces, whole)
         out[...] = total[:, :rows] - split_product(whole[...], top_ref[0], rest_ref[0])
 
     return local_kernel(
         body,
-        [float_array(part, rows), float_array(part, width)],
+        [float_array(part, rows)] + [float_array(part, width)] * (width > rows),
         [own, other, *messages, top, rest],
         flops=6 * part * rows * order,
         scratch=[pltpu.VMEM((part, order), jnp.float32)],
@@ -540,11 +541,11 @@
     for ancestor in range(1, ancestors):
         if ancestor == 1:
             arrived = [send(messages[d - 1], "grp", d) for d in far_first]
-            residual, left = take_messages(solution, others[0], arrived, below_top, below_rest)
+            residual, *left = take_messages(solution, others[0], arrived, below_top, below_rest)
         else:
             pieces = gather_far_first(solutions[-1])
             residual = apply_split(
-                pieces, below_top, below_rest, ancestor - 1, left, (ancestor - 1) * rows
+                pieces, below_top, below_rest, ancestor - 1, left[0], (ancestor - 1) * rows
             )
         pieces = gather_far_first(residual)
         behind = solutions if ancestor + 1 == ancestors else None

time: 136 us -> 134 us (0.985)
  waiting for transfers between devices: 27.7 us -> 22.9 us
  starting transfers between devices: 85.9 us -> 90.2 us
  Pallas kernels: 9.58 us -> 7.54 us
    ppermute x57, waiting for transfers between devices: 23.8 us -> 18.9 us  [send(): return lax.ppermute(value, axis, pairs)]
    ppermute x57, starting transfers between devices: 82.1 us -> 86.6 us  [send(): return lax.ppermute(value, axis, pairs)]
    pallas_call x13, Pallas kernels: 9.58 us -> 7.54 us  [local_kernel(): pl.pallas_call(body, out_shape=list(outs), in_specs=specs or [VMEM] * len...]
  transfers between devices with their start and end apart: 61 -> 61, of which waited for: 27 -> 18; matrix products, arithmetic and copies ran while one was open for 7% -> 7% of each run, Pallas kernels for 3% -> 3%
where the time goes in v22:
time: 134 us
  starting transfers between devices  90.2 us (67%)
  waiting for transfers between devices  22.9 us (17%)
  Pallas kernels  7.54 us (6%)
  matrix products  7.53 us (6%)
  between operations  2.07 us (2%)
  local copies, waits for them, and re-layouts  1.85 us (1%)
  other arithmetic  1.41 us (1%)
    ppermute x57, starting transfers between devices, send(): return lax.ppermute(value, axis, pairs)  86.6 us
    ppermute x57, waiting for transfers between devices, send(): return lax.ppermute(value, axis, pairs)  18.9 us
    pallas_call x13, Pallas kernels, local_kernel(): pl.pallas_call(body, out_shape=list(outs), in_specs=specs or [VMEM] * len...  7.54 us
    dot_general x12, matrix products, contract_last(): lax.dot_general(left, right, (((left.ndim - 1,), (right.ndim - 1,)), ((),...  7.53 us
    ppermute x3, starting transfers between devices, swap(): return lax.ppermute(value, axis, pairs)  3.55 us
    ppermute x3, waiting for transfers between devices, swap(): return lax.ppermute(value, axis, pairs)  2.74 us
  transfers between devices with their start and end apart: 61, of which 18 were waited for; matrix products, arithmetic and copies ran while one was open for 7% of the time, Pallas kernels for 3%

profile of v22, /device:TPU:0, one launch (start us, length us, event | category | flops | bytes accessed | tf_op | source)
XLA Modules:
  0.0 133.6 jit_solution(3664158825497884739)
XLA Ops:
  0.6 1.0 copy-done.2
  1.9 3.1 %collective-permute-start = (f32[64,256]{1,0:T(8,128)S(1)}, f32[64,256]{1,0:T(8,128)S(1)}, u32[]{:S(2)}, u32[]{:S(2)}) collective-permute-start(f32[64,256]{1,0:T(8,128)S(1)} %get-tuple-element.52.refs_0_), channel_id=1, source_target_pairs={{0,1},{1,0},{2,3},{3,2},{4,5},{5,4},{6,7},{7,6},{8,9},{9,8},{10,11... | collective-permute-start | bytes 196616 | tf_op jit(solution)/shard_map/ppermute | solution.py:33
  5.0 2.6 %collective-permute-start.1 = (f32[64,256]{1,0:T(8,128)S(1)}, f32[64,256]{1,0:T(8,128)S(1)}, u32[]{:S(2)}, u32[]{:S(2)}) collective-permute-start(f32[64,256]{1,0:T(8,128)S(1)} %get-tuple-element.52.refs_0_), channel_id=1, source_target_pairs={{0,2},{1,3},{2,0},{3,1},{4,6},{5,7},{6,4},{7,5},{8,10},{9,11},{10,... | collective-permute-start | bytes 196616 | tf_op jit(solution)/shard_map/ppermute | solution.py:33
  7.6 0.9 collective-permute-start.3
  8.5 3.5 %collective-permute-start.4 = (f32[64,256]{1,0:T(8,128)S(1)}, f32[64,256]{1,0:T(8,128)S(1)}, u32[]{:S(2)}, u32[]{:S(2)}) collective-permute-start(f32[64,256]{1,0:T(8,128)S(1)} %get-tuple-element.53.refs_0_), channel_id=1, source_target_pairs={{0,2},{1,3},{2,0},{3,1},{4,6},{5,7},{6,4},{7,5},{8,10},{9,11},{10,... | collective-permute-start | bytes 196616 | tf_op jit(solution)/shard_map/ppermute | solution.py:33
  12.0 1.4 %fusion = (bf16[1,256,1024]{2,1,0:T(8,128)(2,1)S(1)}, bf16[1,256,1024]{2,1,0:T(8,128)(2,1)S(1)}) fusion(f32[1,4,256,1024]{3,2,1,0:T(8,128)} %param.11), kind=kLoop, calls=%fused_computation.2 | loop fusion | flops 1048576 | bytes 2097152 | tf_op jit(solution)/shard_map/convert_element_type | solution.py:487
  14.6 3.0 %collective-permute-start.6 = (f32[64,256]{1,0:T(8,128)S(1)}, f32[64,256]{1,0:T(8,128)S(1)}, u32[]{:S(2)}, u32[]{:S(2)}) collective-permute-start(f32[64,256]{1,0:T(8,128)S(1)} %shard_map.114.refs_0_), channel_id=1, source_target_pairs={{0,1},{1,0},{2,3},{3,2},{4,5},{5,4},{6,7},{7,6},{8,9},{9,8},{10,11... | collective-permute-start | bytes 196616 | tf_op jit(solution)/shard_map/ppermute | solution.py:33
  17.7 2.1 %collective-permute-start.7 = (f32[64,256]{1,0:T(8,128)S(1)}, f32[64,256]{1,0:T(8,128)S(1)}, u32[]{:S(2)}, u32[]{:S(2)}) collective-permute-start(f32[64,256]{1,0:T(8,128)S(1)} %shard_map.114.refs_0_), channel_id=1, source_target_pairs={{0,2},{1,3},{2,0},{3,1},{4,6},{5,7},{6,4},{7,5},{8,10},{9,11},{10,... | collective-permute-start | bytes 196616 | tf_op jit(solution)/shard_map/ppermute | solution.py:33
  19.8 1.4 %collective-permute-start.8 = (f32[64,256]{1,0:T(8,128)S(1)}, f32[64,256]{1,0:T(8,128)S(1)}, u32[]{:S(2)}, u32[]{:S(2)}) collective-permute-start(f32[64,256]{1,0:T(8,128)S(1)} %shard_map.114.refs_0_), channel_id=1, source_target_pairs={{0,3},{1,2},{2,1},{3,0},{4,7},{5,6},{6,5},{7,4},{8,11},{9,10},{10,... | collective-permute-start | bytes 196616 | tf_op jit(solution)/shard_map/ppermute | solution.py:33
  21.7 2.3 %collective-permute-start.9 = (f32[64,256]{1,0:T(8,128)S(1)}, f32[64,256]{1,0:T(8,128)S(1)}, u32[]{:S(2)}, u32[]{:S(2)}) collective-permute-start(f32[64,256]{1,0:T(8,128)S(1)} %shard_map.115.refs_1_), channel_id=1, source_target_pairs={{0,2},{1,3},{2,0},{3,1},{4,6},{5,7},{6,4},{7,5},{8,10},{9,11},{10,... | collective-permute-start | bytes 196616 | tf_op jit(solution)/shard_map/ppermute | solution.py:33
  24.0 0.7 collective-permute-start.13
  24.8 3.1 %collective-permute-done.7 = f32[64,256]{1,0:T(8,128)S(1)} collective-permute-done((f32[64,256]{1,0:T(8,128)S(1)}, f32[64,256]{1,0:T(8,128)S(1)}, u32[]{:S(2)}, u32[]{:S(2)}) %collective-permute-start.7) | collective-permute-done | bytes 65568 | tf_op jit(solution)/shard_map/ppermute | solution.py:33
  28.4 0.6 constant_dynamic-update-slice_fusion.51
  29.0 3.9 %collective-permute-start.11 = (f32[64,256]{1,0:T(8,128)S(1)}, f32[64,256]{1,0:T(8,128)S(1)}, u32[]{:S(2)}, u32[]{:S(2)}) collective-permute-start(f32[64,256]{1,0:T(8,128)S(1)} %get-tuple-element.56), channel_id=1, source_target_pairs={{0,2},{1,3},{2,0},{3,1},{4,6},{5,7},{6,4},{7,5},{8,10},{9,11},{10,... | collective-permute-start | bytes 196616 | tf_op jit(solution)/shard_map/ppermute | solution.py:33
  33.6 0.6 constant_dynamic-update-slice_fusion.43
  34.2 3.8 %collective-permute-start.16 = (f32[64,256]{1,0:T(8,128)S(1)}, f32[64,256]{1,0:T(8,128)S(1)}, u32[]{:S(2)}, u32[]{:S(2)}) collective-permute-start(f32[64,256]{1,0:T(8,128)S(1)} %get-tuple-element.59), channel_id=1, source_target_pairs={{0,2},{1,3},{2,0},{3,1},{4,6},{5,7},{6,4},{7,5},{8,10},{9,11},{10,... | collective-permute-start | bytes 196616 | tf_op jit(solution)/shard_map/ppermute | solution.py:33
  38.7 1.0 collective-permute-done.14
  40.4 2.8 %collective-permute-start.19 = (f32[64,256]{1,0:T(8,128)S(1)}, f32[64,256]{1,0:T(8,128)S(1)}, u32[]{:S(2)}, u32[]{:S(2)}) collective-permute-start(f32[64,256]{1,0:T(8,128)S(1)} %get-tuple-element.61.refs_2_), channel_id=1, source_target_pairs={{0,2},{1,3},{2,0},{3,1},{4,6},{5,7},{6,4},{7,5},{8,10},{9,11},{10,... | collective-permute-start | bytes 196616 | tf_op jit(solution)/shard_map/ppermute | solution.py:33
  43.2 0.7 collective-permute-start.20
  45.0 4.0 %collective-permute-start.21 = (f32[64,256]{1,0:T(8,128)S(1)}, f32[64,256]{1,0:T(8,128)S(1)}, u32[]{:S(2)}, u32[]{:S(2)}) collective-permute-start(f32[64,256]{1,0:T(8,128)S(1)} %get-tuple-element.65.refs_3_), channel_id=1, source_target_pairs={{0,2},{1,3},{2,0},{3,1},{4,6},{5,7},{6,4},{7,5},{8,10},{9,11},{10,... | collective-permute-start | bytes 196616 | tf_op jit(solution)/shard_map/ppermute | solution.py:33
  49.0 1.9 %collective-permute-start.25 = (f32[64,256]{1,0:T(8,128)S(1)}, f32[64,256]{1,0:T(8,128)S(1)}, u32[]{:S(2)}, u32[]{:S(2)}) collective-permute-start(f32[64,256]{1,0:T(8,128)S(1)} %get-tuple-element.65.refs_3_), channel_id=1, source_target_pairs={{0,3},{1,2},{2,1},{3,0},{4,7},{5,6},{6,5},{7,4},{8,11},{9,10},{10,... | collective-permute-start | bytes 196616 | tf_op jit(solution)/shard_map/ppermute | solution.py:33
  51.0 0.6 constant_dynamic-update-slice_fusion.35
  51.6 2.5 %collective-permute-start.23 = (f32[64,256]{1,0:T(8,128)S(1)}, f32[64,256]{1,0:T(8,128)S(1)}, u32[]{:S(2)}, u32[]{:S(2)}) collective-permute-start(f32[64,256]{1,0:T(8,128)S(1)} %get-tuple-element.64), channel_id=1, source_target_pairs={{0,2},{1,3},{2,0},{3,1},{4,6},{5,7},{6,4},{7,5},{8,10},{9,11},{10,... | collective-permute-start | bytes 196616 | tf_op jit(solution)/shard_map/ppermute | solution.py:33
  54.2 1.9 %collective-permute-start.26 = (f32[64,256]{1,0:T(8,128)S(1)}, f32[64,256]{1,0:T(8,128)S(1)}, u32[]{:S(2)}, u32[]{:S(2)}) collective-permute-start(f32[64,256]{1,0:T(8,128)S(1)} %get-tuple-element.64), channel_id=1, source_target_pairs={{0,3},{1,2},{2,1},{3,0},{4,7},{5,6},{6,5},{7,4},{8,11},{9,10},{10,... | collective-permute-start | bytes 196616 | tf_op jit(solution)/shard_map/ppermute | solution.py:33
  56.8 3.6 %collective-permute-start.28 = (f32[64,256]{1,0:T(8,128)S(1)}, f32[64,256]{1,0:T(8,128)S(1)}, u32[]{:S(2)}, u32[]{:S(2)}) collective-permute-start(f32[64,256]{1,0:T(8,128)S(1)} %get-tuple-element.67), channel_id=1, source_target_pairs={{0,2},{1,3},{2,0},{3,1},{4,6},{5,7},{6,4},{7,5},{8,10},{9,11},{10,... | collective-permute-start | bytes 196616 | tf_op jit(solution)/shard_map/ppermute | solution.py:33
  60.4 0.8 collective-permute-start.29
  62.0 3.6 %collective-permute-start.31 = (f32[64,256]{1,0:T(8,128)S(1)}, f32[64,256]{1,0:T(8,128)S(1)}, u32[]{:S(2)}, u32[]{:S(2)}) collective-permute-start(f32[64,256]{1,0:T(8,128)S(1)} %get-tuple-element.69.refs_4_), channel_id=1, source_target_pairs={{0,2},{1,3},{2,0},{3,1},{4,6},{5,7},{6,4},{7,5},{8,10},{9,11},{10,... | collective-permute-start | bytes 196616 | tf_op jit(solution)/shard_map/ppermute | solution.py:33
  65.6 0.8 collective-permute-start.32
  67.6 4.0 %collective-permute-start.33 = (f32[64,256]{1,0:T(8,128)S(1)}, f32[64,256]{1,0:T(8,128)S(1)}, u32[]{:S(2)}, u32[]{:S(2)}) collective-permute-start(f32[64,256]{1,0:T(8,128)S(1)} %get-tuple-element.73.refs_5_), channel_id=1, source_target_pairs={{0,2},{1,3},{2,0},{3,1},{4,6},{5,7},{6,4},{7,5},{8,10},{9,11},{10,... | collective-permute-start | bytes 196616 | tf_op jit(solution)/shard_map/ppermute | solution.py:33
  71.6 1.8 %collective-permute-start.37 = (f32[64,256]{1,0:T(8,128)S(1)}, f32[64,256]{1,0:T(8,128)S(1)}, u32[]{:S(2)}, u32[]{:S(2)}) collective-permute-start(f32[64,256]{1,0:T(8,128)S(1)} %get-tuple-element.73.refs_5_), channel_id=1, source_target_pairs={{0,3},{1,2},{2,1},{3,0},{4,7},{5,6},{6,5},{7,4},{8,11},{9,10},{10,... | collective-permute-start | bytes 196616 | tf_op jit(solution)/shard_map/ppermute | solution.py:33
  73.5 0.6 constant_dynamic-update-slice_fusion.19
  74.2 2.6 %collective-permute-start.35 = (f32[64,256]{1,0:T(8,128)S(1)}, f32[64,256]{1,0:T(8,128)S(1)}, u32[]{:S(2)}, u32[]{:S(2)}) collective-permute-start(f32[64,256]{1,0:T(8,128)S(1)} %get-tuple-element.72), channel_id=1, source_target_pairs={{0,2},{1,3},{2,0},{3,1},{4,6},{5,7},{6,4},{7,5},{8,10},{9,11},{10,... | collective-permute-start | bytes 196616 | tf_op jit(solution)/shard_map/ppermute | solution.py:33
  76.8 1.8 %collective-permute-start.38 = (f32[64,256]{1,0:T(8,128)S(1)}, f32[64,256]{1,0:T(8,128)S(1)}, u32[]{:S(2)}, u32[]{:S(2)}) collective-permute-start(f32[64,256]{1,0:T(8,128)S(1)} %get-tuple-element.72), channel_id=1, source_target_pairs={{0,3},{1,2},{2,1},{3,0},{4,7},{5,6},{6,5},{7,4},{8,11},{9,10},{10,... | collective-permute-start | bytes 196616 | tf_op jit(solution)/shard_map/ppermute | solution.py:33
  79.3 2.6 %collective-permute-start.40 = (f32[64,256]{1,0:T(8,128)S(1)}, f32[64,256]{1,0:T(8,128)S(1)}, u32[]{:S(2)}, u32[]{:S(2)}) collective-permute-start(f32[64,256]{1,0:T(8,128)S(1)} %get-tuple-element.75), channel_id=1, source_target_pairs={{0,2},{1,3},{2,0},{3,1},{4,6},{5,7},{6,4},{7,5},{8,10},{9,11},{10,... | collective-permute-start | bytes 196616 | tf_op jit(solution)/shard_map/ppermute | solution.py:33
  82.0 1.8 %collective-permute-start.41 = (f32[64,256]{1,0:T(8,128)S(1)}, f32[64,256]{1,0:T(8,128)S(1)}, u32[]{:S(2)}, u32[]{:S(2)}) collective-permute-start(f32[64,256]{1,0:T(8,128)S(1)} %get-tuple-element.75), channel_id=1, source_target_pairs={{0,3},{1,2},{2,1},{3,0},{4,7},{5,6},{6,5},{7,4},{8,11},{9,10},{10,... | collective-permute-start | bytes 196616 | tf_op jit(solution)/shard_map/ppermute | solution.py:33
  84.5 4.2 %collective-permute-start.43 = (f32[64,256]{1,0:T(8,128)S(1)}, f32[64,256]{1,0:T(8,128)S(1)}, u32[]{:S(2)}, u32[]{:S(2)}) collective-permute-start(f32[64,256]{1,0:T(8,128)S(1)} %get-tuple-element.77.refs_6_), channel_id=1, source_target_pairs={{0,2},{1,3},{2,0},{3,1},{4,6},{5,7},{6,4},{7,5},{8,10},{9,11},{10,... | collective-permute-start | bytes 196616 | tf_op jit(solution)/shard_map/ppermute | solution.py:33
  88.7 1.4 %collective-permute-start.44 = (f32[64,256]{1,0:T(8,128)S(1)}, f32[64,256]{1,0:T(8,128)S(1)}, u32[]{:S(2)}, u32[]{:S(2)}) collective-permute-start(f32[64,256]{1,0:T(8,128)S(1)} %get-tuple-element.77.refs_6_), channel_id=1, source_target_pairs={{0,3},{1,2},{2,1},{3,0},{4,7},{5,6},{6,5},{7,4},{8,11},{9,10},{10,... | collective-permute-start | bytes 196616 | tf_op jit(solution)/shard_map/ppermute | solution.py:33
  90.9 3.1 %collective-permute-start.46 = (f32[64,256]{1,0:T(8,128)S(1)}, f32[64,256]{1,0:T(8,128)S(1)}, u32[]{:S(2)}, u32[]{:S(2)}) collective-permute-start(f32[64,256]{1,0:T(8,128)S(1)} %get-tuple-element.79.refs_7_), channel_id=1, source_target_pairs={{0,2},{1,3},{2,0},{3,1},{4,6},{5,7},{6,4},{7,5},{8,10},{9,11},{10,... | collective-permute-start | bytes 196616 | tf_op jit(solution)/shard_map/ppermute | solution.py:33
  93.9 1.4 %collective-permute-start.47 = (f32[64,256]{1,0:T(8,128)S(1)}, f32[64,256]{1,0:T(8,128)S(1)}, u32[]{:S(2)}, u32[]{:S(2)}) collective-permute-start(f32[64,256]{1,0:T(8,128)S(1)} %get-tuple-element.79.refs_7_), channel_id=1, source_target_pairs={{0,3},{1,2},{2,1},{3,0},{4,7},{5,6},{6,5},{7,4},{8,11},{9,10},{10,... | collective-permute-start | bytes 196616 | tf_op jit(solution)/shard_map/ppermute | solution.py:33
  95.4 1.0 collective-permute-done.46
  96.4 1.2 shard_map.117.refs_0_
  97.6 2.7 %collective-permute-done.45 = f32[64,256]{1,0:T(8,128)S(1)} collective-permute-done((f32[64,256]{1,0:T(8,128)S(1)}, f32[64,256]{1,0:T(8,128)S(1)}, u32[]{:S(2)}, u32[]{:S(2)}) %collective-permute-start.45) | collective-permute-done | bytes 65568 | tf_op jit(solution)/shard_map/ppermute | solution.py:33
  100.3 1.2 shard_map.118
  101.6 1.3 collective-permute-done.48.refs_1_
  103.0 2.5 %collective-permute-start.49 = (f32[2,16,512]{2,1,0:T(8,128)S(1)}, f32[2,16,512]{2,1,0:T(8,128)S(1)}, u32[]{:S(2)}, u32[]{:S(2)}) collective-permute-start(f32[2,16,512]{2,1,0:T(8,128)S(1)} %get-tuple-element.85), channel_id=1, source_target_pairs={{0,24},{4,28},{8,16},{12,20},{16,8},{20,12},{24,0},{28,4},{1,25},{... | collective-permute-start | bytes 196616 | tf_op jit(solution)/shard_map/ppermute | solution.py:81
  106.5 1.0 shard_map.119
  107.5 0.7 collective-permute-done.49.refs_1_
  108.2 1.5 %collective-permute-done.50.refs_2_ = f32[2,16,512]{2,1,0:T(8,128)S(1)} collective-permute-done((f32[2,16,512]{2,1,0:T(8,128)S(1)}, f32[2,16,512]{2,1,0:T(8,128)S(1)}, u32[]{:S(2)}, u32[]{:S(2)}) %collective-permute-start.50) | collective-permute-done | bytes 65568 | tf_op jit(solution)/shard_map/ppermute | solution.py:81
  110.7 1.0 collective-permute-start.52
  111.7 1.4 %collective-permute-start.53 = (f32[16,1024]{1,0:T(8,128)S(1)}, f32[16,1024]{1,0:T(8,128)S(1)}, u32[]{:S(2)}, u32[]{:S(2)}) collective-permute-start(f32[16,1024]{1,0:T(8,128)S(1)} %get-tuple-element.89.refs_2_.refs_0_), channel_id=1, source_target_pairs={{0,3},{1,2},{2,1},{3,0},{4,7},{5,6},{6,5},{7,4},{8,11},{9,10},{10,... | collective-permute-start | bytes 196616 | tf_op jit(solution)/shard_map/ppermute | solution.py:33
  113.1 1.1 collective-permute-start.54
  114.7 1.8 %collective-permute-done.52.refs_1_ = f32[16,1024]{1,0:T(8,128)S(1)} collective-permute-done((f32[16,1024]{1,0:T(8,128)S(1)}, f32[16,1024]{1,0:T(8,128)S(1)}, u32[]{:S(2)}, u32[]{:S(2)}) %collective-permute-start.52) | collective-permute-done | bytes 65568 | tf_op jit(solution)/shard_map/ppermute | solution.py:33
  116.5 1.5 %collective-permute-done.53.refs_2_ = f32[16,1024]{1,0:T(8,128)S(1)} collective-permute-done((f32[16,1024]{1,0:T(8,128)S(1)}, f32[16,1024]{1,0:T(8,128)S(1)}, u32[]{:S(2)}, u32[]{:S(2)}) %collective-permute-start.53) | collective-permute-done | bytes 65568 | tf_op jit(solution)/shard_map/ppermute | solution.py:33
  118.4 1.2 collective-permute-start.55
  119.7 1.6 %collective-permute-start.56 = (f32[16,512]{1,0:T(8,128)S(1)}, f32[16,512]{1,0:T(8,128)S(1)}, u32[]{:S(2)}, u32[]{:S(2)}) collective-permute-start(f32[16,512]{1,0:T(8,128)S(1)} %get-tuple-element.98), channel_id=1, source_target_pairs={{0,3},{1,2},{2,1},{3,0},{4,7},{5,6},{6,5},{7,4},{8,11},{9,10},{10,... | collective-permute-start | bytes 98312 | tf_op jit(solution)/shard_map/ppermute | solution.py:33
  121.3 0.7 collective-permute-start.57
  122.0 1.5 %collective-permute-done.55.refs_2_ = f32[16,512]{1,0:T(8,128)S(1)} collective-permute-done((f32[16,512]{1,0:T(8,128)S(1)}, f32[16,512]{1,0:T(8,128)S(1)}, u32[]{:S(2)}, u32[]{:S(2)}) %collective-permute-start.55) | collective-permute-done | bytes 32800 | tf_op jit(solution)/shard_map/ppermute | solution.py:33
  123.5 2.0 %collective-permute-done.56.refs_3_ = f32[16,512]{1,0:T(8,128)S(1)} collective-permute-done((f32[16,512]{1,0:T(8,128)S(1)}, f32[16,512]{1,0:T(8,128)S(1)}, u32[]{:S(2)}, u32[]{:S(2)}) %collective-permute-start.56) | collective-permute-done | bytes 32800 | tf_op jit(solution)/shard_map/ppermute | solution.py:33
  125.9 1.0 collective-permute-start.58
  126.9 1.7 %collective-permute-start.59 = (f32[16,256]{1,0:T(8,128)S(1)}, f32[16,256]{1,0:T(8,128)S(1)}, u32[]{:S(2)}, u32[]{:S(2)}) collective-permute-start(f32[16,256]{1,0:T(8,128)S(1)} %shard_map.124.refs_0_), channel_id=1, source_target_pairs={{0,3},{1,2},{2,1},{3,0},{4,7},{5,6},{6,5},{7,4},{8,11},{9,10},{10,... | collective-permute-start | bytes 49160 | tf_op jit(solution)/shard_map/ppermute | solution.py:33
  128.6 0.8 collective-permute-start.60
  129.4 1.1 collective-permute-done.58.refs_1_
  130.6 2.0 %collective-permute-done.59.refs_2_ = f32[16,256]{1,0:T(8,128)S(1)} collective-permute-done((f32[16,256]{1,0:T(8,128)S(1)}, f32[16,256]{1,0:T(8,128)S(1)}, u32[]{:S(2)}, u32[]{:S(2)}) %collective-permute-start.59) | collective-permute-done | bytes 16416 | tf_op jit(solution)/shard_map/ppermute | solution.py:33
  132.6 1.0 shard_map.125
  (162 shorter events, 13.1 us)
Async XLA Ops:
  1.7 26.2 %copy-start.3 = (f32[1,4,256,128]{3,2,1,0:T(8,128)S(1)}, f32[1,4,256,128]{3,2,1,0:T(8,128)}, u32[]{:S(2)}) copy-start(f32[1,4,256,128]{3,2,1,0:T(8,128)} %rhs_ref.3) | copy-start | bytes 1572868
  1.9 10.1 %collective-permute-start = (f32[64,256]{1,0:T(8,128)S(1)}, f32[64,256]{1,0:T(8,128)S(1)}, u32[]{:S(2)}, u32[]{:S(2)}) collective-permute-start(f32[64,256]{1,0:T(8,128)S(1)} %get-tuple-element.52.refs_0_), channel_id=1, source_target_pairs={{0,1},{1,0},{2,3},{3,2},{4,5},{5,4},{6,7},{7,6},{8,9},{9,8},{10,11... | collective-permute-start | bytes 196616 | tf_op jit(solution)/shard_map/ppermute | solution.py:33
  5.0 9.1 %collective-permute-start.1 = (f32[64,256]{1,0:T(8,128)S(1)}, f32[64,256]{1,0:T(8,128)S(1)}, u32[]{:S(2)}, u32[]{:S(2)}) collective-permute-start(f32[64,256]{1,0:T(8,128)S(1)} %get-tuple-element.52.refs_0_), channel_id=1, source_target_pairs={{0,2},{1,3},{2,0},{3,1},{4,6},{5,7},{6,4},{7,5},{8,10},{9,11},{10,... | collective-permute-start | bytes 196616 | tf_op jit(solution)/shard_map/ppermute | solution.py:33
  7.6 6.6 %collective-permute-start.2 = (f32[64,256]{1,0:T(8,128)S(1)}, f32[64,256]{1,0:T(8,128)S(1)}, u32[]{:S(2)}, u32[]{:S(2)}) collective-permute-start(f32[64,256]{1,0:T(8,128)S(1)} %get-tuple-element.52.refs_0_), channel_id=1, source_target_pairs={{0,3},{1,2},{2,1},{3,0},{4,7},{5,6},{6,5},{7,4},{8,11},{9,10},{10,... | collective-permute-start | bytes 196616 | tf_op jit(solution)/shard_map/ppermute | solution.py:33
  7.6 12.2 %collective-permute-start.3 = (f32[64,256]{1,0:T(8,128)S(1)}, f32[64,256]{1,0:T(8,128)S(1)}, u32[]{:S(2)}, u32[]{:S(2)}) collective-permute-start(f32[64,256]{1,0:T(8,128)S(1)} %get-tuple-element.53.refs_0_), channel_id=1, source_target_pairs={{0,1},{1,0},{2,3},{3,2},{4,5},{5,4},{6,7},{7,6},{8,9},{9,8},{10,11... | collective-permute-start | bytes 196616 | tf_op jit(solution)/shard_map/ppermute | solution.py:33
  8.5 12.7 %collective-permute-start.4 = (f32[64,256]{1,0:T(8,128)S(1)}, f32[64,256]{1,0:T(8,128)S(1)}, u32[]{:S(2)}, u32[]{:S(2)}) collective-permute-start(f32[64,256]{1,0:T(8,128)S(1)} %get-tuple-element.53.refs_0_), channel_id=1, source_target_pairs={{0,2},{1,3},{2,0},{3,1},{4,6},{5,7},{6,4},{7,5},{8,10},{9,11},{10,... | collective-permute-start | bytes 196616 | tf_op jit(solution)/shard_map/ppermute | solution.py:33
  12.0 9.2 %collective-permute-start.5 = (f32[64,256]{1,0:T(8,128)S(1)}, f32[64,256]{1,0:T(8,128)S(1)}, u32[]{:S(2)}, u32[]{:S(2)}) collective-permute-start(f32[64,256]{1,0:T(8,128)S(1)} %get-tuple-element.53.refs_0_), channel_id=1, source_target_pairs={{0,3},{1,2},{2,1},{3,0},{4,7},{5,6},{6,5},{7,4},{8,11},{9,10},{10,... | collective-permute-start | bytes 196616 | tf_op jit(solution)/shard_map/ppermute | solution.py:33
  14.6 13.2 %collective-permute-start.6 = (f32[64,256]{1,0:T(8,128)S(1)}, f32[64,256]{1,0:T(8,128)S(1)}, u32[]{:S(2)}, u32[]{:S(2)}) collective-permute-start(f32[64,256]{1,0:T(8,128)S(1)} %shard_map.114.refs_0_), channel_id=1, source_target_pairs={{0,1},{1,0},{2,3},{3,2},{4,5},{5,4},{6,7},{7,6},{8,9},{9,8},{10,11... | collective-permute-start | bytes 196616 | tf_op jit(solution)/shard_map/ppermute | solution.py:33
  17.7 10.2 %collective-permute-start.7 = (f32[64,256]{1,0:T(8,128)S(1)}, f32[64,256]{1,0:T(8,128)S(1)}, u32[]{:S(2)}, u32[]{:S(2)}) collective-permute-start(f32[64,256]{1,0:T(8,128)S(1)} %shard_map.114.refs_0_), channel_id=1, source_target_pairs={{0,2},{1,3},{2,0},{3,1},{4,6},{5,7},{6,4},{7,5},{8,10},{9,11},{10,... | collective-permute-start | bytes 196616 | tf_op jit(solution)/shard_map/ppermute | solution.py:33
  19.8 8.5 %collective-permute-start.8 = (f32[64,256]{1,0:T(8,128)S(1)}, f32[64,256]{1,0:T(8,128)S(1)}, u32[]{:S(2)}, u32[]{:S(2)}) collective-permute-start(f32[64,256]{1,0:T(8,128)S(1)} %shard_map.114.refs_0_), channel_id=1, source_target_pairs={{0,3},{1,2},{2,1},{3,0},{4,7},{5,6},{6,5},{7,4},{8,11},{9,10},{10,... | collective-permute-start | bytes 196616 | tf_op jit(solution)/shard_map/ppermute | solution.py:33
  21.7 11.8 %collective-permute-start.9 = (f32[64,256]{1,0:T(8,128)S(1)}, f32[64,256]{1,0:T(8,128)S(1)}, u32[]{:S(2)}, u32[]{:S(2)}) collective-permute-start(f32[64,256]{1,0:T(8,128)S(1)} %shard_map.115.refs_1_), channel_id=1, source_target_pairs={{0,2},{1,3},{2,0},{3,1},{4,6},{5,7},{6,4},{7,5},{8,10},{9,11},{10,... | collective-permute-start | bytes 196616 | tf_op jit(solution)/shard_map/ppermute | solution.py:33
  24.0 9.6 %collective-permute-start.13 = (f32[64,256]{1,0:T(8,128)S(1)}, f32[64,256]{1,0:T(8,128)S(1)}, u32[]{:S(2)}, u32[]{:S(2)}) collective-permute-start(f32[64,256]{1,0:T(8,128)S(1)} %shard_map.115.refs_1_), channel_id=1, source_target_pairs={{0,3},{1,2},{2,1},{3,0},{4,7},{5,6},{6,5},{7,4},{8,11},{9,10},{10,... | collective-permute-start | bytes 196616 | tf_op jit(solution)/shard_map/ppermute | solution.py:33
  27.9 5.6 %collective-permute-start.12 = (f32[64,256]{1,0:T(8,128)S(1)}, f32[64,256]{1,0:T(8,128)S(1)}, u32[]{:S(2)}, u32[]{:S(2)}) collective-permute-start(f32[64,256]{1,0:T(8,128)S(1)} %shard_map.115.refs_1_), channel_id=1, source_target_pairs={{0,1},{1,0},{2,3},{3,2},{4,5},{5,4},{6,7},{7,6},{8,9},{9,8},{10,11... | collective-permute-start | bytes 196616 | tf_op jit(solution)/shard_map/ppermute | solution.py:33
  29.0 9.6 %collective-permute-start.11 = (f32[64,256]{1,0:T(8,128)S(1)}, f32[64,256]{1,0:T(8,128)S(1)}, u32[]{:S(2)}, u32[]{:S(2)}) collective-permute-start(f32[64,256]{1,0:T(8,128)S(1)} %get-tuple-element.56), channel_id=1, source_target_pairs={{0,2},{1,3},{2,0},{3,1},{4,6},{5,7},{6,4},{7,5},{8,10},{9,11},{10,... | collective-permute-start | bytes 196616 | tf_op jit(solution)/shard_map/ppermute | solution.py:33
  32.9 6.8 %collective-permute-start.14 = (f32[64,256]{1,0:T(8,128)S(1)}, f32[64,256]{1,0:T(8,128)S(1)}, u32[]{:S(2)}, u32[]{:S(2)}) collective-permute-start(f32[64,256]{1,0:T(8,128)S(1)} %get-tuple-element.56), channel_id=1, source_target_pairs={{0,3},{1,2},{2,1},{3,0},{4,7},{5,6},{6,5},{7,4},{8,11},{9,10},{10,... | collective-permute-start | bytes 196616 | tf_op jit(solution)/shard_map/ppermute | solution.py:33
  33.4 5.2 %collective-permute-start.10 = (f32[64,256]{1,0:T(8,128)S(1)}, f32[64,256]{1,0:T(8,128)S(1)}, u32[]{:S(2)}, u32[]{:S(2)}) collective-permute-start(f32[64,256]{1,0:T(8,128)S(1)} %get-tuple-element.56), channel_id=1, source_target_pairs={{0,1},{1,0},{2,3},{3,2},{4,5},{5,4},{6,7},{7,6},{8,9},{9,8},{10,11... | collective-permute-start | bytes 196616 | tf_op jit(solution)/shard_map/ppermute | solution.py:33
  34.2 9.7 %collective-permute-start.16 = (f32[64,256]{1,0:T(8,128)S(1)}, f32[64,256]{1,0:T(8,128)S(1)}, u32[]{:S(2)}, u32[]{:S(2)}) collective-permute-start(f32[64,256]{1,0:T(8,128)S(1)} %get-tuple-element.59), channel_id=1, source_target_pairs={{0,2},{1,3},{2,0},{3,1},{4,6},{5,7},{6,4},{7,5},{8,10},{9,11},{10,... | collective-permute-start | bytes 196616 | tf_op jit(solution)/shard_map/ppermute | solution.py:33
  38.0 6.3 %collective-permute-start.17 = (f32[64,256]{1,0:T(8,128)S(1)}, f32[64,256]{1,0:T(8,128)S(1)}, u32[]{:S(2)}, u32[]{:S(2)}) collective-permute-start(f32[64,256]{1,0:T(8,128)S(1)} %get-tuple-element.59), channel_id=1, source_target_pairs={{0,3},{1,2},{2,1},{3,0},{4,7},{5,6},{6,5},{7,4},{8,11},{9,10},{10,... | collective-permute-start | bytes 196616 | tf_op jit(solution)/shard_map/ppermute | solution.py:33
  38.6 5.7 %collective-permute-start.15 = (f32[64,256]{1,0:T(8,128)S(1)}, f32[64,256]{1,0:T(8,128)S(1)}, u32[]{:S(2)}, u32[]{:S(2)}) collective-permute-start(f32[64,256]{1,0:T(8,128)S(1)} %get-tuple-element.59), channel_id=1, source_target_pairs={{0,1},{1,0},{2,3},{3,2},{4,5},{5,4},{6,7},{7,6},{8,9},{9,8},{10,11... | collective-permute-start | bytes 196616 | tf_op jit(solution)/shard_map/ppermute | solution.py:33
  40.4 10.5 %collective-permute-start.19 = (f32[64,256]{1,0:T(8,128)S(1)}, f32[64,256]{1,0:T(8,128)S(1)}, u32[]{:S(2)}, u32[]{:S(2)}) collective-permute-start(f32[64,256]{1,0:T(8,128)S(1)} %get-tuple-element.61.refs_2_), channel_id=1, source_target_pairs={{0,2},{1,3},{2,0},{3,1},{4,6},{5,7},{6,4},{7,5},{8,10},{9,11},{10,... | collective-permute-start | bytes 196616 | tf_op jit(solution)/shard_map/ppermute | solution.py:33
  43.2 7.7 %collective-permute-start.20 = (f32[64,256]{1,0:T(8,128)S(1)}, f32[64,256]{1,0:T(8,128)S(1)}, u32[]{:S(2)}, u32[]{:S(2)}) collective-permute-start(f32[64,256]{1,0:T(8,128)S(1)} %get-tuple-element.61.refs_2_), channel_id=1, source_target_pairs={{0,3},{1,2},{2,1},{3,0},{4,7},{5,6},{6,5},{7,4},{8,11},{9,10},{10,... | collective-permute-start | bytes 196616 | tf_op jit(solution)/shard_map/ppermute | solution.py:33
  43.9 7.0 %collective-permute-start.18 = (f32[64,256]{1,0:T(8,128)S(1)}, f32[64,256]{1,0:T(8,128)S(1)}, u32[]{:S(2)}, u32[]{:S(2)}) collective-permute-start(f32[64,256]{1,0:T(8,128)S(1)} %get-tuple-element.61.refs_2_), channel_id=1, source_target_pairs={{0,1},{1,0},{2,3},{3,2},{4,5},{5,4},{6,7},{7,6},{8,9},{9,8},{10,11... | collective-permute-start | bytes 196616 | tf_op jit(solution)/shard_map/ppermute | solution.py:33
  45.0 11.0 %collective-permute-start.21 = (f32[64,256]{1,0:T(8,128)S(1)}, f32[64,256]{1,0:T(8,128)S(1)}, u32[]{:S(2)}, u32[]{:S(2)}) collective-permute-start(f32[64,256]{1,0:T(8,128)S(1)} %get-tuple-element.65.refs_3_), channel_id=1, source_target_pairs={{0,2},{1,3},{2,0},{3,1},{4,6},{5,7},{6,4},{7,5},{8,10},{9,11},{10,... | collective-permute-start | bytes 196616 | tf_op jit(solution)/shard_map/ppermute | solution.py:33
  49.0 7.1 %collective-permute-start.25 = (f32[64,256]{1,0:T(8,128)S(1)}, f32[64,256]{1,0:T(8,128)S(1)}, u32[]{:S(2)}, u32[]{:S(2)}) collective-permute-start(f32[64,256]{1,0:T(8,128)S(1)} %get-tuple-element.65.refs_3_), channel_id=1, source_target_pairs={{0,3},{1,2},{2,1},{3,0},{4,7},{5,6},{6,5},{7,4},{8,11},{9,10},{10,... | collective-permute-start | bytes 196616 | tf_op jit(solution)/shard_map/ppermute | solution.py:33
  50.9 5.2 %collective-permute-start.24 = (f32[64,256]{1,0:T(8,128)S(1)}, f32[64,256]{1,0:T(8,128)S(1)}, u32[]{:S(2)}, u32[]{:S(2)}) collective-permute-start(f32[64,256]{1,0:T(8,128)S(1)} %get-tuple-element.65.refs_3_), channel_id=1, source_target_pairs={{0,1},{1,0},{2,3},{3,2},{4,5},{5,4},{6,7},{7,6},{8,9},{9,8},{10,11... | collective-permute-start | bytes 196616 | tf_op jit(solution)/shard_map/ppermute | solution.py:33
  51.6 9.6 %collective-permute-start.23 = (f32[64,256]{1,0:T(8,128)S(1)}, f32[64,256]{1,0:T(8,128)S(1)}, u32[]{:S(2)}, u32[]{:S(2)}) collective-permute-start(f32[64,256]{1,0:T(8,128)S(1)} %get-tuple-element.64), channel_id=1, source_target_pairs={{0,2},{1,3},{2,0},{3,1},{4,6},{5,7},{6,4},{7,5},{8,10},{9,11},{10,... | collective-permute-start | bytes 196616 | tf_op jit(solution)/shard_map/ppermute | solution.py:33
  54.2 7.1 %collective-permute-start.26 = (f32[64,256]{1,0:T(8,128)S(1)}, f32[64,256]{1,0:T(8,128)S(1)}, u32[]{:S(2)}, u32[]{:S(2)}) collective-permute-start(f32[64,256]{1,0:T(8,128)S(1)} %get-tuple-element.64), channel_id=1, source_target_pairs={{0,3},{1,2},{2,1},{3,0},{4,7},{5,6},{6,5},{7,4},{8,11},{9,10},{10,... | collective-permute-start | bytes 196616 | tf_op jit(solution)/shard_map/ppermute | solution.py:33
  56.1 5.2 %collective-permute-start.22 = (f32[64,256]{1,0:T(8,128)S(1)}, f32[64,256]{1,0:T(8,128)S(1)}, u32[]{:S(2)}, u32[]{:S(2)}) collective-permute-start(f32[64,256]{1,0:T(8,128)S(1)} %get-tuple-element.64), channel_id=1, source_target_pairs={{0,1},{1,0},{2,3},{3,2},{4,5},{5,4},{6,7},{7,6},{8,9},{9,8},{10,11... | collective-permute-start | bytes 196616 | tf_op jit(solution)/shard_map/ppermute | solution.py:33
  56.8 9.6 %collective-permute-start.28 = (f32[64,256]{1,0:T(8,128)S(1)}, f32[64,256]{1,0:T(8,128)S(1)}, u32[]{:S(2)}, u32[]{:S(2)}) collective-permute-start(f32[64,256]{1,0:T(8,128)S(1)} %get-tuple-element.67), channel_id=1, source_target_pairs={{0,2},{1,3},{2,0},{3,1},{4,6},{5,7},{6,4},{7,5},{8,10},{9,11},{10,... | collective-permute-start | bytes 196616 | tf_op jit(solution)/shard_map/ppermute | solution.py:33
  60.4 6.5 %collective-permute-start.29 = (f32[64,256]{1,0:T(8,128)S(1)}, f32[64,256]{1,0:T(8,128)S(1)}, u32[]{:S(2)}, u32[]{:S(2)}) collective-permute-start(f32[64,256]{1,0:T(8,128)S(1)} %get-tuple-element.67), channel_id=1, source_target_pairs={{0,3},{1,2},{2,1},{3,0},{4,7},{5,6},{6,5},{7,4},{8,11},{9,10},{10,... | collective-permute-start | bytes 196616 | tf_op jit(solution)/shard_map/ppermute | solution.py:33
  61.3 5.7 %collective-permute-start.27 = (f32[64,256]{1,0:T(8,128)S(1)}, f32[64,256]{1,0:T(8,128)S(1)}, u32[]{:S(2)}, u32[]{:S(2)}) collective-permute-start(f32[64,256]{1,0:T(8,128)S(1)} %get-tuple-element.67), channel_id=1, source_target_pairs={{0,1},{1,0},{2,3},{3,2},{4,5},{5,4},{6,7},{7,6},{8,9},{9,8},{10,11... | collective-permute-start | bytes 196616 | tf_op jit(solution)/shard_map/ppermute | solution.py:33
  62.0 11.4 %collective-permute-start.31 = (f32[64,256]{1,0:T(8,128)S(1)}, f32[64,256]{1,0:T(8,128)S(1)}, u32[]{:S(2)}, u32[]{:S(2)}) collective-permute-start(f32[64,256]{1,0:T(8,128)S(1)} %get-tuple-element.69.refs_4_), channel_id=1, source_target_pairs={{0,2},{1,3},{2,0},{3,1},{4,6},{5,7},{6,4},{7,5},{8,10},{9,11},{10,... | collective-permute-start | bytes 196616 | tf_op jit(solution)/shard_map/ppermute | solution.py:33
  65.6 7.9 %collective-permute-start.32 = (f32[64,256]{1,0:T(8,128)S(1)}, f32[64,256]{1,0:T(8,128)S(1)}, u32[]{:S(2)}, u32[]{:S(2)}) collective-permute-start(f32[64,256]{1,0:T(8,128)S(1)} %get-tuple-element.69.refs_4_), channel_id=1, source_target_pairs={{0,3},{1,2},{2,1},{3,0},{4,7},{5,6},{6,5},{7,4},{8,11},{9,10},{10,... | collective-permute-start | bytes 196616 | tf_op jit(solution)/shard_map/ppermute | solution.py:33
  66.4 7.0 %collective-permute-start.30 = (f32[64,256]{1,0:T(8,128)S(1)}, f32[64,256]{1,0:T(8,128)S(1)}, u32[]{:S(2)}, u32[]{:S(2)}) collective-permute-start(f32[64,256]{1,0:T(8,128)S(1)} %get-tuple-element.69.refs_4_), channel_id=1, source_target_pairs={{0,1},{1,0},{2,3},{3,2},{4,5},{5,4},{6,7},{7,6},{8,9},{9,8},{10,11... | collective-permute-start | bytes 196616 | tf_op jit(solution)/shard_map/ppermute | solution.py:33
  67.6 11.0 %collective-permute-start.33 = (f32[64,256]{1,0:T(8,128)S(1)}, f32[64,256]{1,0:T(8,128)S(1)}, u32[]{:S(2)}, u32[]{:S(2)}) collective-permute-start(f32[64,256]{1,0:T(8,128)S(1)} %get-tuple-element.73.refs_5_), channel_id=1, source_target_pairs={{0,2},{1,3},{2,0},{3,1},{4,6},{5,7},{6,4},{7,5},{8,10},{9,11},{10,... | collective-permute-start | bytes 196616 | tf_op jit(solution)/shard_map/ppermute | solution.py:33
  71.6 7.1 %collective-permute-start.37 = (f32[64,256]{1,0:T(8,128)S(1)}, f32[64,256]{1,0:T(8,128)S(1)}, u32[]{:S(2)}, u32[]{:S(2)}) collective-permute-start(f32[64,256]{1,0:T(8,128)S(1)} %get-tuple-element.73.refs_5_), channel_id=1, source_target_pairs={{0,3},{1,2},{2,1},{3,0},{4,7},{5,6},{6,5},{7,4},{8,11},{9,10},{10,... | collective-permute-start | bytes 196616 | tf_op jit(solution)/shard_map/ppermute | solution.py:33
  73.4 5.2 %collective-permute-start.36 = (f32[64,256]{1,0:T(8,128)S(1)}, f32[64,256]{1,0:T(8,128)S(1)}, u32[]{:S(2)}, u32[]{:S(2)}) collective-permute-start(f32[64,256]{1,0:T(8,128)S(1)} %get-tuple-element.73.refs_5_), channel_id=1, source_target_pairs={{0,1},{1,0},{2,3},{3,2},{4,5},{5,4},{6,7},{7,6},{8,9},{9,8},{10,11... | collective-permute-start | bytes 196616 | tf_op jit(solution)/shard_map/ppermute | solution.py:33
  74.2 9.6 %collective-permute-start.35 = (f32[64,256]{1,0:T(8,128)S(1)}, f32[64,256]{1,0:T(8,128)S(1)}, u32[]{:S(2)}, u32[]{:S(2)}) collective-permute-start(f32[64,256]{1,0:T(8,128)S(1)} %get-tuple-element.72), channel_id=1, source_target_pairs={{0,2},{1,3},{2,0},{3,1},{4,6},{5,7},{6,4},{7,5},{8,10},{9,11},{10,... | collective-permute-start | bytes 196616 | tf_op jit(solution)/shard_map/ppermute | solution.py:33
  76.8 7.1 %collective-permute-start.38 = (f32[64,256]{1,0:T(8,128)S(1)}, f32[64,256]{1,0:T(8,128)S(1)}, u32[]{:S(2)}, u32[]{:S(2)}) collective-permute-start(f32[64,256]{1,0:T(8,128)S(1)} %get-tuple-element.72), channel_id=1, source_target_pairs={{0,3},{1,2},{2,1},{3,0},{4,7},{5,6},{6,5},{7,4},{8,11},{9,10},{10,... | collective-permute-start | bytes 196616 | tf_op jit(solution)/shard_map/ppermute | solution.py:33
  78.6 5.2 %collective-permute-start.34 = (f32[64,256]{1,0:T(8,128)S(1)}, f32[64,256]{1,0:T(8,128)S(1)}, u32[]{:S(2)}, u32[]{:S(2)}) collective-permute-start(f32[64,256]{1,0:T(8,128)S(1)} %get-tuple-element.72), channel_id=1, source_target_pairs={{0,1},{1,0},{2,3},{3,2},{4,5},{5,4},{6,7},{7,6},{8,9},{9,8},{10,11... | collective-permute-start | bytes 196616 | tf_op jit(solution)/shard_map/ppermute | solution.py:33
  79.3 10.8 %collective-permute-start.40 = (f32[64,256]{1,0:T(8,128)S(1)}, f32[64,256]{1,0:T(8,128)S(1)}, u32[]{:S(2)}, u32[]{:S(2)}) collective-permute-start(f32[64,256]{1,0:T(8,128)S(1)} %get-tuple-element.75), channel_id=1, source_target_pairs={{0,2},{1,3},{2,0},{3,1},{4,6},{5,7},{6,4},{7,5},{8,10},{9,11},{10,... | collective-permute-start | bytes 196616 | tf_op jit(solution)/shard_map/ppermute | solution.py:33
  82.0 8.2 %collective-permute-start.41 = (f32[64,256]{1,0:T(8,128)S(1)}, f32[64,256]{1,0:T(8,128)S(1)}, u32[]{:S(2)}, u32[]{:S(2)}) collective-permute-start(f32[64,256]{1,0:T(8,128)S(1)} %get-tuple-element.75), channel_id=1, source_target_pairs={{0,3},{1,2},{2,1},{3,0},{4,7},{5,6},{6,5},{7,4},{8,11},{9,10},{10,... | collective-permute-start | bytes 196616 | tf_op jit(solution)/shard_map/ppermute | solution.py:33
  83.8 6.3 %collective-permute-start.39 = (f32[64,256]{1,0:T(8,128)S(1)}, f32[64,256]{1,0:T(8,128)S(1)}, u32[]{:S(2)}, u32[]{:S(2)}) collective-permute-start(f32[64,256]{1,0:T(8,128)S(1)} %get-tuple-element.75), channel_id=1, source_target_pairs={{0,1},{1,0},{2,3},{3,2},{4,5},{5,4},{6,7},{7,6},{8,9},{9,8},{10,11... | collective-permute-start | bytes 196616 | tf_op jit(solution)/shard_map/ppermute | solution.py:33
  84.5 10.8 %collective-permute-start.43 = (f32[64,256]{1,0:T(8,128)S(1)}, f32[64,256]{1,0:T(8,128)S(1)}, u32[]{:S(2)}, u32[]{:S(2)}) collective-permute-start(f32[64,256]{1,0:T(8,128)S(1)} %get-tuple-element.77.refs_6_), channel_id=1, source_target_pairs={{0,2},{1,3},{2,0},{3,1},{4,6},{5,7},{6,4},{7,5},{8,10},{9,11},{10,... | collective-permute-start | bytes 196616 | tf_op jit(solution)/shard_map/ppermute | solution.py:33
  88.7 6.6 %collective-permute-start.44 = (f32[64,256]{1,0:T(8,128)S(1)}, f32[64,256]{1,0:T(8,128)S(1)}, u32[]{:S(2)}, u32[]{:S(2)}) collective-permute-start(f32[64,256]{1,0:T(8,128)S(1)} %get-tuple-element.77.refs_6_), channel_id=1, source_target_pairs={{0,3},{1,2},{2,1},{3,0},{4,7},{5,6},{6,5},{7,4},{8,11},{9,10},{10,... | collective-permute-start | bytes 196616 | tf_op jit(solution)/shard_map/ppermute | solution.py:33
  90.1 5.2 %collective-permute-start.42 = (f32[64,256]{1,0:T(8,128)S(1)}, f32[64,256]{1,0:T(8,128)S(1)}, u32[]{:S(2)}, u32[]{:S(2)}) collective-permute-start(f32[64,256]{1,0:T(8,128)S(1)} %get-tuple-element.77.refs_6_), channel_id=1, source_target_pairs={{0,1},{1,0},{2,3},{3,2},{4,5},{5,4},{6,7},{7,6},{8,9},{9,8},{10,11... | collective-permute-start | bytes 196616 | tf_op jit(solution)/shard_map/ppermute | solution.py:33
  90.9 5.5 %collective-permute-start.46 = (f32[64,256]{1,0:T(8,128)S(1)}, f32[64,256]{1,0:T(8,128)S(1)}, u32[]{:S(2)}, u32[]{:S(2)}) collective-permute-start(f32[64,256]{1,0:T(8,128)S(1)} %get-tuple-element.79.refs_7_), channel_id=1, source_target_pairs={{0,2},{1,3},{2,0},{3,1},{4,6},{5,7},{6,4},{7,5},{8,10},{9,11},{10,... | collective-permute-start | bytes 196616 | tf_op jit(solution)/shard_map/ppermute | solution.py:33
  93.9 6.4 %collective-permute-start.47 = (f32[64,256]{1,0:T(8,128)S(1)}, f32[64,256]{1,0:T(8,128)S(1)}, u32[]{:S(2)}, u32[]{:S(2)}) collective-permute-start(f32[64,256]{1,0:T(8,128)S(1)} %get-tuple-element.79.refs_7_), channel_id=1, source_target_pairs={{0,3},{1,2},{2,1},{3,0},{4,7},{5,6},{6,5},{7,4},{8,11},{9,10},{10,... | collective-permute-start | bytes 196616 | tf_op jit(solution)/shard_map/ppermute | solution.py:33
  95.3 5.0 %collective-permute-start.45 = (f32[64,256]{1,0:T(8,128)S(1)}, f32[64,256]{1,0:T(8,128)S(1)}, u32[]{:S(2)}, u32[]{:S(2)}) collective-permute-start(f32[64,256]{1,0:T(8,128)S(1)} %get-tuple-element.79.refs_7_), channel_id=1, source_target_pairs={{0,1},{1,0},{2,3},{3,2},{4,5},{5,4},{6,7},{7,6},{8,9},{9,8},{10,11... | collective-permute-start | bytes 196616 | tf_op jit(solution)/shard_map/ppermute | solution.py:33
  96.3 17.9 %copy-start.1 = (f32[2,256,1024]{2,1,0:T(8,128)S(1)}, f32[2,256,1024]{2,1,0:T(8,128)}, u32[]{:S(2)}) copy-start(f32[2,256,1024]{2,1,0:T(8,128)} %refs_0_.1) | copy-start | bytes 6291460
  96.4 17.9 %copy-start.4 = (f32[1,256,1024]{2,1,0:T(8,128)S(1)}, f32[1,256,1024]{2,1,0:T(8,128)}, u32[]{:S(2)}) copy-start(f32[1,256,1024]{2,1,0:T(8,128)} %refs_1_.1) | copy-start | bytes 3145732
  101.5 1.4 %collective-permute-start.48 = (f32[4,16,512]{2,1,0:T(8,128)S(1)}, f32[4,16,512]{2,1,0:T(8,128)S(1)}, u32[]{:S(2)}, u32[]{:S(2)}) collective-permute-start(f32[4,16,512]{2,1,0:T(8,128)S(1)} %get-tuple-element.83), channel_id=1, source_target_pairs={{0,4},{4,0},{8,12},{12,8},{16,20},{20,16},{24,28},{28,24},{1,5},{5... | collective-permute-start | bytes 393224 | tf_op jit(solution)/shard_map/ppermute | solution.py:281
  103.0 5.3 %collective-permute-start.49 = (f32[2,16,512]{2,1,0:T(8,128)S(1)}, f32[2,16,512]{2,1,0:T(8,128)S(1)}, u32[]{:S(2)}, u32[]{:S(2)}) collective-permute-start(f32[2,16,512]{2,1,0:T(8,128)S(1)} %get-tuple-element.85), channel_id=1, source_target_pairs={{0,24},{4,28},{8,16},{12,20},{16,8},{20,12},{24,0},{28,4},{1,25},{... | collective-permute-start | bytes 196616 | tf_op jit(solution)/shard_map/ppermute | solution.py:81
  105.5 4.3 %collective-permute-start.50 = (f32[2,16,512]{2,1,0:T(8,128)S(1)}, f32[2,16,512]{2,1,0:T(8,128)S(1)}, u32[]{:S(2)}, u32[]{:S(2)}) collective-permute-start(f32[2,16,512]{2,1,0:T(8,128)S(1)} %get-tuple-element.86), channel_id=1, source_target_pairs={{0,16},{4,20},{8,24},{12,28},{16,0},{20,4},{24,8},{28,12},{1,17},{... | collective-permute-start | bytes 196616 | tf_op jit(solution)/shard_map/ppermute | solution.py:81
  106.0 4.3 %collective-permute-start.51 = (f32[2,16,512]{2,1,0:T(8,128)S(1)}, f32[2,16,512]{2,1,0:T(8,128)S(1)}, u32[]{:S(2)}, u32[]{:S(2)}) collective-permute-start(f32[2,16,512]{2,1,0:T(8,128)S(1)} %get-tuple-element.87), channel_id=1, source_target_pairs={{0,8},{4,12},{8,0},{12,4},{16,24},{20,28},{24,16},{28,20},{1,9},{5... | collective-permute-start | bytes 196616 | tf_op jit(solution)/shard_map/ppermute | solution.py:81
  110.7 5.8 %collective-permute-start.52 = (f32[16,1024]{1,0:T(8,128)S(1)}, f32[16,1024]{1,0:T(8,128)S(1)}, u32[]{:S(2)}, u32[]{:S(2)}) collective-permute-start(f32[16,1024]{1,0:T(8,128)S(1)} %get-tuple-element.89.refs_2_.refs_0_), channel_id=1, source_target_pairs={{0,2},{1,3},{2,0},{3,1},{4,6},{5,7},{6,4},{7,5},{8,10},{9,11},{10,... | collective-permute-start | bytes 196616 | tf_op jit(solution)/shard_map/ppermute | solution.py:33
  111.7 6.2 %collective-permute-start.53 = (f32[16,1024]{1,0:T(8,128)S(1)}, f32[16,1024]{1,0:T(8,128)S(1)}, u32[]{:S(2)}, u32[]{:S(2)}) collective-permute-start(f32[16,1024]{1,0:T(8,128)S(1)} %get-tuple-element.89.refs_2_.refs_0_), channel_id=1, source_target_pairs={{0,3},{1,2},{2,1},{3,0},{4,7},{5,6},{6,5},{7,4},{8,11},{9,10},{10,... | collective-permute-start | bytes 196616 | tf_op jit(solution)/shard_map/ppermute | solution.py:33
  113.1 5.0 %collective-permute-start.54 = (f32[16,1024]{1,0:T(8,128)S(1)}, f32[16,1024]{1,0:T(8,128)S(1)}, u32[]{:S(2)}, u32[]{:S(2)}) collective-permute-start(f32[16,1024]{1,0:T(8,128)S(1)} %get-tuple-element.89.refs_2_.refs_0_), channel_id=1, source_target_pairs={{0,1},{1,0},{2,3},{3,2},{4,5},{5,4},{6,7},{7,6},{8,9},{9,8},{10,11... | collective-permute-start | bytes 196616 | tf_op jit(solution)/shard_map/ppermute | solution.py:33
  118.4 5.1 %collective-permute-start.55 = (f32[16,512]{1,0:T(8,128)S(1)}, f32[16,512]{1,0:T(8,128)S(1)}, u32[]{:S(2)}, u32[]{:S(2)}) collective-permute-start(f32[16,512]{1,0:T(8,128)S(1)} %get-tuple-element.97), channel_id=1, source_target_pairs={{0,2},{1,3},{2,0},{3,1},{4,6},{5,7},{6,4},{7,5},{8,10},{9,11},{10,... | collective-permute-start | bytes 98312 | tf_op jit(solution)/shard_map/ppermute | solution.py:33
  119.7 5.9 %collective-permute-start.56 = (f32[16,512]{1,0:T(8,128)S(1)}, f32[16,512]{1,0:T(8,128)S(1)}, u32[]{:S(2)}, u32[]{:S(2)}) collective-permute-start(f32[16,512]{1,0:T(8,128)S(1)} %get-tuple-element.98), channel_id=1, source_target_pairs={{0,3},{1,2},{2,1},{3,0},{4,7},{5,6},{6,5},{7,4},{8,11},{9,10},{10,... | collective-permute-start | bytes 98312 | tf_op jit(solution)/shard_map/ppermute | solution.py:33
  121.3 4.3 %collective-permute-start.57 = (f32[16,512]{1,0:T(8,128)S(1)}, f32[16,512]{1,0:T(8,128)S(1)}, u32[]{:S(2)}, u32[]{:S(2)}) collective-permute-start(f32[16,512]{1,0:T(8,128)S(1)} %get-tuple-element.99), channel_id=1, source_target_pairs={{0,1},{1,0},{2,3},{3,2},{4,5},{5,4},{6,7},{7,6},{8,9},{9,8},{10,11... | collective-permute-start | bytes 98312 | tf_op jit(solution)/shard_map/ppermute | solution.py:33
  125.9 4.7 %collective-permute-start.58 = (f32[16,256]{1,0:T(8,128)S(1)}, f32[16,256]{1,0:T(8,128)S(1)}, u32[]{:S(2)}, u32[]{:S(2)}) collective-permute-start(f32[16,256]{1,0:T(8,128)S(1)} %shard_map.124.refs_0_), channel_id=1, source_target_pairs={{0,2},{1,3},{2,0},{3,1},{4,6},{5,7},{6,4},{7,5},{8,10},{9,11},{10,... | collective-permute-start | bytes 49160 | tf_op jit(solution)/shard_map/ppermute | solution.py:33
  126.9 5.6 %collective-permute-start.59 = (f32[16,256]{1,0:T(8,128)S(1)}, f32[16,256]{1,0:T(8,128)S(1)}, u32[]{:S(2)}, u32[]{:S(2)}) collective-permute-start(f32[16,256]{1,0:T(8,128)S(1)} %shard_map.124.refs_0_), channel_id=1, source_target_pairs={{0,3},{1,2},{2,1},{3,0},{4,7},{5,6},{6,5},{7,4},{8,11},{9,10},{10,... | collective-permute-start | bytes 49160 | tf_op jit(solution)/shard_map/ppermute | solution.py:33
  128.6 3.9 %collective-permute-start.60 = (f32[16,256]{1,0:T(8,128)S(1)}, f32[16,256]{1,0:T(8,128)S(1)}, u32[]{:S(2)}, u32[]{:S(2)}) collective-permute-start(f32[16,256]{1,0:T(8,128)S(1)} %shard_map.124.refs_0_), channel_id=1, source_target_pairs={{0,1},{1,0},{2,3},{3,2},{4,5},{5,4},{6,7},{7,6},{8,9},{9,8},{10,11... | collective-permute-start | bytes 49160 | tf_op jit(solution)/shard_map/ppermute | solution.py:33
  (7 other events, 95.4 us)

commit v23 on v22

--- a/solution.py
+++ b/solution.py
@@ -33,18 +33,20 @@
     return lax.ppermute(value, axis, pairs)
 
 
-def gather_rows(value, ties=(), far_first=False):
+def gather_rows(value, ties=None, far_first=False):
     members = lax.axis_size("grp")
     me = lax.axis_index("grp")
     rows = value.shape[1]
     pieces = [(me * rows, value)]
     distances = list(range(1, members))
+    if ties is not None:
+        distances[1:] = distances[:0:-1]
     if far_first:
         distances = distances[1:] + distances[:1]
     for distance in distances:
         owner = partner(me, distance, members)
         tied = value
-        if distance in dict(ties):
+        if distance in dict(ties or ()):
             tied = lax.optimization_barrier((value, dict(ties)[distance]))[0]
         pieces.append((owner * rows, send(tied, "grp", distance)))
     return pieces
@@ -502,7 +504,7 @@
                 pieces[2] = (offset, lax.optimization_barrier((piece, last[1]))[0])
             if step == 0:
                 owned = apply_split(
-                    [p for _, p in pieces],
+                    [p for _, p in pieces[:2] + pieces[:1:-1]],
                     first_top,
                     first_rest,
                     0,

time: 134 us -> 134 us (level)
  waiting for transfers between devices: 22.9 us -> 24.8 us
    ppermute x57, waiting for transfers between devices: 18.9 us -> 20.8 us  [send(): return lax.ppermute(value, axis, pairs)]
  transfers between devices with their start and end apart: 61 -> 61, of which waited for: 18 -> 25; matrix products, arithmetic and copies ran while one was open for 7% -> 7% of each run, Pallas kernels for 3% -> 3%
where the time goes in v23:
time: 134 us
  starting transfers between devices  89 us (66%)
  waiting for transfers between devices  24.8 us (19%)
  Pallas kernels  7.53 us (6%)
  matrix products  7.53 us (6%)
  between operations  1.95 us (1%)
  local copies, waits for them, and re-layouts  1.78 us (1%)
  other arithmetic  1.41 us (1%)
    ppermute x57, starting transfers between devices, send(): return lax.ppermute(value, axis, pairs)  85.4 us
    ppermute x57, waiting for transfers between devices, send(): return lax.ppermute(value, axis, pairs)  20.8 us
    dot_general x12, matrix products, contract_last(): lax.dot_general(left, right, (((left.ndim - 1,), (right.ndim - 1,)), ((),...  7.53 us
    pallas_call x13, Pallas kernels, local_kernel(): pl.pallas_call(body, out_shape=list(outs), in_specs=specs or [VMEM] * len...  7.53 us
    ppermute x3, starting transfers between devices, swap(): return lax.ppermute(value, axis, pairs)  3.55 us
    ppermute x3, waiting for transfers between devices, swap(): return lax.ppermute(value, axis, pairs)  2.74 us
  transfers between devices with their start and end apart: 61, of which 25 were waited for; matrix products, arithmetic and copies ran while one was open for 7% of the time, Pallas kernels for 3%

profile of v23, /device:TPU:0, one launch (start us, length us, event | category | flops | bytes accessed | tf_op | source)
XLA Modules:
  0.0 134.0 jit_solution(6649196628971440571)
XLA Ops:
  0.6 1.0 copy-done.2
  1.9 3.1 %collective-permute-start = (f32[64,256]{1,0:T(8,128)S(1)}, f32[64,256]{1,0:T(8,128)S(1)}, u32[]{:S(2)}, u32[]{:S(2)}) collective-permute-start(f32[64,256]{1,0:T(8,128)S(1)} %get-tuple-element.52.refs_0_), channel_id=1, source_target_pairs={{0,1},{1,0},{2,3},{3,2},{4,5},{5,4},{6,7},{7,6},{8,9},{9,8},{10,11... | collective-permute-start | bytes 196616 | tf_op jit(solution)/shard_map/ppermute | solution.py:33
  5.0 2.6 %collective-permute-start.1 = (f32[64,256]{1,0:T(8,128)S(1)}, f32[64,256]{1,0:T(8,128)S(1)}, u32[]{:S(2)}, u32[]{:S(2)}) collective-permute-start(f32[64,256]{1,0:T(8,128)S(1)} %get-tuple-element.52.refs_0_), channel_id=1, source_target_pairs={{0,2},{1,3},{2,0},{3,1},{4,6},{5,7},{6,4},{7,5},{8,10},{9,11},{10,... | collective-permute-start | bytes 196616 | tf_op jit(solution)/shard_map/ppermute | solution.py:33
  7.6 0.9 collective-permute-start.3
  8.5 3.5 %collective-permute-start.4 = (f32[64,256]{1,0:T(8,128)S(1)}, f32[64,256]{1,0:T(8,128)S(1)}, u32[]{:S(2)}, u32[]{:S(2)}) collective-permute-start(f32[64,256]{1,0:T(8,128)S(1)} %get-tuple-element.53.refs_0_), channel_id=1, source_target_pairs={{0,2},{1,3},{2,0},{3,1},{4,6},{5,7},{6,4},{7,5},{8,10},{9,11},{10,... | collective-permute-start | bytes 196616 | tf_op jit(solution)/shard_map/ppermute | solution.py:33
  12.0 1.4 %fusion = (bf16[1,256,1024]{2,1,0:T(8,128)(2,1)S(1)}, bf16[1,256,1024]{2,1,0:T(8,128)(2,1)S(1)}) fusion(f32[1,4,256,1024]{3,2,1,0:T(8,128)} %param.11), kind=kLoop, calls=%fused_computation.2 | loop fusion | flops 1048576 | bytes 2097152 | tf_op jit(solution)/shard_map/convert_element_type | solution.py:489
  14.6 3.0 %collective-permute-start.6 = (f32[64,256]{1,0:T(8,128)S(1)}, f32[64,256]{1,0:T(8,128)S(1)}, u32[]{:S(2)}, u32[]{:S(2)}) collective-permute-start(f32[64,256]{1,0:T(8,128)S(1)} %shard_map.114.refs_0_), channel_id=1, source_target_pairs={{0,1},{1,0},{2,3},{3,2},{4,5},{5,4},{6,7},{7,6},{8,9},{9,8},{10,11... | collective-permute-start | bytes 196616 | tf_op jit(solution)/shard_map/ppermute | solution.py:33
  17.7 3.5 %collective-permute-start.7 = (f32[64,256]{1,0:T(8,128)S(1)}, f32[64,256]{1,0:T(8,128)S(1)}, u32[]{:S(2)}, u32[]{:S(2)}) collective-permute-start(f32[64,256]{1,0:T(8,128)S(1)} %shard_map.114.refs_0_), channel_id=1, source_target_pairs={{0,3},{1,2},{2,1},{3,0},{4,7},{5,6},{6,5},{7,4},{8,11},{9,10},{10,... | collective-permute-start | bytes 196616 | tf_op jit(solution)/shard_map/ppermute | solution.py:33
  21.7 1.8 %collective-permute-start.9 = (f32[64,256]{1,0:T(8,128)S(1)}, f32[64,256]{1,0:T(8,128)S(1)}, u32[]{:S(2)}, u32[]{:S(2)}) collective-permute-start(f32[64,256]{1,0:T(8,128)S(1)} %shard_map.115.refs_1_), channel_id=1, source_target_pairs={{0,3},{1,2},{2,1},{3,0},{4,7},{5,6},{6,5},{7,4},{8,11},{9,10},{10,... | collective-permute-start | bytes 196616 | tf_op jit(solution)/shard_map/ppermute | solution.py:33
  23.5 2.0 %collective-permute-start.13 = (f32[64,256]{1,0:T(8,128)S(1)}, f32[64,256]{1,0:T(8,128)S(1)}, u32[]{:S(2)}, u32[]{:S(2)}) collective-permute-start(f32[64,256]{1,0:T(8,128)S(1)} %shard_map.115.refs_1_), channel_id=1, source_target_pairs={{0,2},{1,3},{2,0},{3,1},{4,6},{5,7},{6,4},{7,5},{8,10},{9,11},{10,... | collective-permute-start | bytes 196616 | tf_op jit(solution)/shard_map/ppermute | solution.py:33
  25.6 0.8 collective-permute-start.12
  26.7 1.5 %collective-permute-done.8 = f32[64,256]{1,0:T(8,128)S(1)} collective-permute-done((f32[64,256]{1,0:T(8,128)S(1)}, f32[64,256]{1,0:T(8,128)S(1)}, u32[]{:S(2)}, u32[]{:S(2)}) %collective-permute-start.8) | collective-permute-done | bytes 65568 | tf_op jit(solution)/shard_map/ppermute | solution.py:33
  28.2 0.6 constant_dynamic-update-slice_fusion.51
  28.9 2.5 %collective-permute-start.11 = (f32[64,256]{1,0:T(8,128)S(1)}, f32[64,256]{1,0:T(8,128)S(1)}, u32[]{:S(2)}, u32[]{:S(2)}) collective-permute-start(f32[64,256]{1,0:T(8,128)S(1)} %get-tuple-element.56), channel_id=1, source_target_pairs={{0,3},{1,2},{2,1},{3,0},{4,7},{5,6},{6,5},{7,4},{8,11},{9,10},{10,... | collective-permute-start | bytes 196616 | tf_op jit(solution)/shard_map/ppermute | solution.py:33
  31.4 1.9 %collective-permute-start.10 = (f32[64,256]{1,0:T(8,128)S(1)}, f32[64,256]{1,0:T(8,128)S(1)}, u32[]{:S(2)}, u32[]{:S(2)}) collective-permute-start(f32[64,256]{1,0:T(8,128)S(1)} %get-tuple-element.56), channel_id=1, source_target_pairs={{0,1},{1,0},{2,3},{3,2},{4,5},{5,4},{6,7},{7,6},{8,9},{9,8},{10,11... | collective-permute-start | bytes 196616 | tf_op jit(solution)/shard_map/ppermute | solution.py:33
  33.4 0.6 constant_dynamic-update-slice_fusion.43
  34.1 2.5 %collective-permute-start.16 = (f32[64,256]{1,0:T(8,128)S(1)}, f32[64,256]{1,0:T(8,128)S(1)}, u32[]{:S(2)}, u32[]{:S(2)}) collective-permute-start(f32[64,256]{1,0:T(8,128)S(1)} %get-tuple-element.59), channel_id=1, source_target_pairs={{0,3},{1,2},{2,1},{3,0},{4,7},{5,6},{6,5},{7,4},{8,11},{9,10},{10,... | collective-permute-start | bytes 196616 | tf_op jit(solution)/shard_map/ppermute | solution.py:33
  36.6 1.9 %collective-permute-start.15 = (f32[64,256]{1,0:T(8,128)S(1)}, f32[64,256]{1,0:T(8,128)S(1)}, u32[]{:S(2)}, u32[]{:S(2)}) collective-permute-start(f32[64,256]{1,0:T(8,128)S(1)} %get-tuple-element.59), channel_id=1, source_target_pairs={{0,1},{1,0},{2,3},{3,2},{4,5},{5,4},{6,7},{7,6},{8,9},{9,8},{10,11... | collective-permute-start | bytes 196616 | tf_op jit(solution)/shard_map/ppermute | solution.py:33
  38.8 0.6 constant_dynamic-update-slice_fusion.39
  39.4 2.5 %collective-permute-start.19 = (f32[64,256]{1,0:T(8,128)S(1)}, f32[64,256]{1,0:T(8,128)S(1)}, u32[]{:S(2)}, u32[]{:S(2)}) collective-permute-start(f32[64,256]{1,0:T(8,128)S(1)} %get-tuple-element.61.refs_2_), channel_id=1, source_target_pairs={{0,3},{1,2},{2,1},{3,0},{4,7},{5,6},{6,5},{7,4},{8,11},{9,10},{10,... | collective-permute-start | bytes 196616 | tf_op jit(solution)/shard_map/ppermute | solution.py:33
  41.9 1.9 %collective-permute-start.18 = (f32[64,256]{1,0:T(8,128)S(1)}, f32[64,256]{1,0:T(8,128)S(1)}, u32[]{:S(2)}, u32[]{:S(2)}) collective-permute-start(f32[64,256]{1,0:T(8,128)S(1)} %get-tuple-element.61.refs_2_), channel_id=1, source_target_pairs={{0,1},{1,0},{2,3},{3,2},{4,5},{5,4},{6,7},{7,6},{8,9},{9,8},{10,11... | collective-permute-start | bytes 196616 | tf_op jit(solution)/shard_map/ppermute | solution.py:33
  44.4 0.6 constant_dynamic-update-slice_fusion.33
  45.0 2.5 %collective-permute-start.21 = (f32[64,256]{1,0:T(8,128)S(1)}, f32[64,256]{1,0:T(8,128)S(1)}, u32[]{:S(2)}, u32[]{:S(2)}) collective-permute-start(f32[64,256]{1,0:T(8,128)S(1)} %get-tuple-element.65.refs_3_), channel_id=1, source_target_pairs={{0,3},{1,2},{2,1},{3,0},{4,7},{5,6},{6,5},{7,4},{8,11},{9,10},{10,... | collective-permute-start | bytes 196616 | tf_op jit(solution)/shard_map/ppermute | solution.py:33
  47.6 1.9 %collective-permute-start.24 = (f32[64,256]{1,0:T(8,128)S(1)}, f32[64,256]{1,0:T(8,128)S(1)}, u32[]{:S(2)}, u32[]{:S(2)}) collective-permute-start(f32[64,256]{1,0:T(8,128)S(1)} %get-tuple-element.65.refs_3_), channel_id=1, source_target_pairs={{0,1},{1,0},{2,3},{3,2},{4,5},{5,4},{6,7},{7,6},{8,9},{9,8},{10,11... | collective-permute-start | bytes 196616 | tf_op jit(solution)/shard_map/ppermute | solution.py:33
  50.0 0.6 constant_dynamic-update-slice_fusion.35
  50.6 2.5 %collective-permute-start.23 = (f32[64,256]{1,0:T(8,128)S(1)}, f32[64,256]{1,0:T(8,128)S(1)}, u32[]{:S(2)}, u32[]{:S(2)}) collective-permute-start(f32[64,256]{1,0:T(8,128)S(1)} %get-tuple-element.64), channel_id=1, source_target_pairs={{0,3},{1,2},{2,1},{3,0},{4,7},{5,6},{6,5},{7,4},{8,11},{9,10},{10,... | collective-permute-start | bytes 196616 | tf_op jit(solution)/shard_map/ppermute | solution.py:33
  53.2 1.9 %collective-permute-start.22 = (f32[64,256]{1,0:T(8,128)S(1)}, f32[64,256]{1,0:T(8,128)S(1)}, u32[]{:S(2)}, u32[]{:S(2)}) collective-permute-start(f32[64,256]{1,0:T(8,128)S(1)} %get-tuple-element.64), channel_id=1, source_target_pairs={{0,1},{1,0},{2,3},{3,2},{4,5},{5,4},{6,7},{7,6},{8,9},{9,8},{10,11... | collective-permute-start | bytes 196616 | tf_op jit(solution)/shard_map/ppermute | solution.py:33
  55.6 0.6 constant_dynamic-update-slice_fusion.27
  56.3 2.5 %collective-permute-start.28 = (f32[64,256]{1,0:T(8,128)S(1)}, f32[64,256]{1,0:T(8,128)S(1)}, u32[]{:S(2)}, u32[]{:S(2)}) collective-permute-start(f32[64,256]{1,0:T(8,128)S(1)} %get-tuple-element.67), channel_id=1, source_target_pairs={{0,3},{1,2},{2,1},{3,0},{4,7},{5,6},{6,5},{7,4},{8,11},{9,10},{10,... | collective-permute-start | bytes 196616 | tf_op jit(solution)/shard_map/ppermute | solution.py:33
  58.8 1.9 %collective-permute-start.27 = (f32[64,256]{1,0:T(8,128)S(1)}, f32[64,256]{1,0:T(8,128)S(1)}, u32[]{:S(2)}, u32[]{:S(2)}) collective-permute-start(f32[64,256]{1,0:T(8,128)S(1)} %get-tuple-element.67), channel_id=1, source_target_pairs={{0,1},{1,0},{2,3},{3,2},{4,5},{5,4},{6,7},{7,6},{8,9},{9,8},{10,11... | collective-permute-start | bytes 196616 | tf_op jit(solution)/shard_map/ppermute | solution.py:33
  61.9 2.5 %collective-permute-start.31 = (f32[64,256]{1,0:T(8,128)S(1)}, f32[64,256]{1,0:T(8,128)S(1)}, u32[]{:S(2)}, u32[]{:S(2)}) collective-permute-start(f32[64,256]{1,0:T(8,128)S(1)} %get-tuple-element.69.refs_4_), channel_id=1, source_target_pairs={{0,3},{1,2},{2,1},{3,0},{4,7},{5,6},{6,5},{7,4},{8,11},{9,10},{10,... | collective-permute-start | bytes 196616 | tf_op jit(solution)/shard_map/ppermute | solution.py:33
  64.4 1.9 %collective-permute-start.30 = (f32[64,256]{1,0:T(8,128)S(1)}, f32[64,256]{1,0:T(8,128)S(1)}, u32[]{:S(2)}, u32[]{:S(2)}) collective-permute-start(f32[64,256]{1,0:T(8,128)S(1)} %get-tuple-element.69.refs_4_), channel_id=1, source_target_pairs={{0,1},{1,0},{2,3},{3,2},{4,5},{5,4},{6,7},{7,6},{8,9},{9,8},{10,11... | collective-permute-start | bytes 196616 | tf_op jit(solution)/shard_map/ppermute | solution.py:33
  67.5 2.5 %collective-permute-start.33 = (f32[64,256]{1,0:T(8,128)S(1)}, f32[64,256]{1,0:T(8,128)S(1)}, u32[]{:S(2)}, u32[]{:S(2)}) collective-permute-start(f32[64,256]{1,0:T(8,128)S(1)} %get-tuple-element.73.refs_5_), channel_id=1, source_target_pairs={{0,3},{1,2},{2,1},{3,0},{4,7},{5,6},{6,5},{7,4},{8,11},{9,10},{10,... | collective-permute-start | bytes 196616 | tf_op jit(solution)/shard_map/ppermute | solution.py:33
  70.0 1.9 %collective-permute-start.36 = (f32[64,256]{1,0:T(8,128)S(1)}, f32[64,256]{1,0:T(8,128)S(1)}, u32[]{:S(2)}, u32[]{:S(2)}) collective-permute-start(f32[64,256]{1,0:T(8,128)S(1)} %get-tuple-element.73.refs_5_), channel_id=1, source_target_pairs={{0,1},{1,0},{2,3},{3,2},{4,5},{5,4},{6,7},{7,6},{8,9},{9,8},{10,11... | collective-permute-start | bytes 196616 | tf_op jit(solution)/shard_map/ppermute | solution.py:33
  73.1 2.5 %collective-permute-start.35 = (f32[64,256]{1,0:T(8,128)S(1)}, f32[64,256]{1,0:T(8,128)S(1)}, u32[]{:S(2)}, u32[]{:S(2)}) collective-permute-start(f32[64,256]{1,0:T(8,128)S(1)} %get-tuple-element.72), channel_id=1, source_target_pairs={{0,3},{1,2},{2,1},{3,0},{4,7},{5,6},{6,5},{7,4},{8,11},{9,10},{10,... | collective-permute-start | bytes 196616 | tf_op jit(solution)/shard_map/ppermute | solution.py:33
  75.6 1.9 %collective-permute-start.34 = (f32[64,256]{1,0:T(8,128)S(1)}, f32[64,256]{1,0:T(8,128)S(1)}, u32[]{:S(2)}, u32[]{:S(2)}) collective-permute-start(f32[64,256]{1,0:T(8,128)S(1)} %get-tuple-element.72), channel_id=1, source_target_pairs={{0,1},{1,0},{2,3},{3,2},{4,5},{5,4},{6,7},{7,6},{8,9},{9,8},{10,11... | collective-permute-start | bytes 196616 | tf_op jit(solution)/shard_map/ppermute | solution.py:33
  78.1 0.6 constant_dynamic-update-slice_fusion.11
  78.7 2.5 %collective-permute-start.40 = (f32[64,256]{1,0:T(8,128)S(1)}, f32[64,256]{1,0:T(8,128)S(1)}, u32[]{:S(2)}, u32[]{:S(2)}) collective-permute-start(f32[64,256]{1,0:T(8,128)S(1)} %get-tuple-element.75), channel_id=1, source_target_pairs={{0,3},{1,2},{2,1},{3,0},{4,7},{5,6},{6,5},{7,4},{8,11},{9,10},{10,... | collective-permute-start | bytes 196616 | tf_op jit(solution)/shard_map/ppermute | solution.py:33
  81.3 1.9 %collective-permute-start.39 = (f32[64,256]{1,0:T(8,128)S(1)}, f32[64,256]{1,0:T(8,128)S(1)}, u32[]{:S(2)}, u32[]{:S(2)}) collective-permute-start(f32[64,256]{1,0:T(8,128)S(1)} %get-tuple-element.75), channel_id=1, source_target_pairs={{0,1},{1,0},{2,3},{3,2},{4,5},{5,4},{6,7},{7,6},{8,9},{9,8},{10,11... | collective-permute-start | bytes 196616 | tf_op jit(solution)/shard_map/ppermute | solution.py:33
  84.3 2.5 %collective-permute-start.43 = (f32[64,256]{1,0:T(8,128)S(1)}, f32[64,256]{1,0:T(8,128)S(1)}, u32[]{:S(2)}, u32[]{:S(2)}) collective-permute-start(f32[64,256]{1,0:T(8,128)S(1)} %get-tuple-element.77.refs_6_), channel_id=1, source_target_pairs={{0,3},{1,2},{2,1},{3,0},{4,7},{5,6},{6,5},{7,4},{8,11},{9,10},{10,... | collective-permute-start | bytes 196616 | tf_op jit(solution)/shard_map/ppermute | solution.py:33
  86.9 1.9 %collective-permute-start.42 = (f32[64,256]{1,0:T(8,128)S(1)}, f32[64,256]{1,0:T(8,128)S(1)}, u32[]{:S(2)}, u32[]{:S(2)}) collective-permute-start(f32[64,256]{1,0:T(8,128)S(1)} %get-tuple-element.77.refs_6_), channel_id=1, source_target_pairs={{0,1},{1,0},{2,3},{3,2},{4,5},{5,4},{6,7},{7,6},{8,9},{9,8},{10,11... | collective-permute-start | bytes 196616 | tf_op jit(solution)/shard_map/ppermute | solution.py:33
  88.8 3.3 %collective-permute-done.41 = f32[64,256]{1,0:T(8,128)S(1)} collective-permute-done((f32[64,256]{1,0:T(8,128)S(1)}, f32[64,256]{1,0:T(8,128)S(1)}, u32[]{:S(2)}, u32[]{:S(2)}) %collective-permute-start.41) | collective-permute-done | bytes 65568 | tf_op jit(solution)/shard_map/ppermute | solution.py:33
  92.9 4.3 %collective-permute-start.45 = (f32[64,256]{1,0:T(8,128)S(1)}, f32[64,256]{1,0:T(8,128)S(1)}, u32[]{:S(2)}, u32[]{:S(2)}) collective-permute-start(f32[64,256]{1,0:T(8,128)S(1)} %get-tuple-element.79.refs_7_), channel_id=1, source_target_pairs={{0,1},{1,0},{2,3},{3,2},{4,5},{5,4},{6,7},{7,6},{8,9},{9,8},{10,11... | collective-permute-start | bytes 196616 | tf_op jit(solution)/shard_map/ppermute | solution.py:33
  97.3 1.6 %collective-permute-done.46 = f32[64,256]{1,0:T(8,128)S(1)} collective-permute-done((f32[64,256]{1,0:T(8,128)S(1)}, f32[64,256]{1,0:T(8,128)S(1)}, u32[]{:S(2)}, u32[]{:S(2)}) %collective-permute-start.46) | collective-permute-done | bytes 65568 | tf_op jit(solution)/shard_map/ppermute | solution.py:33
  98.9 1.2 shard_map.117.refs_0_
  100.2 1.2 shard_map.118
  101.5 1.3 collective-permute-done.48.refs_1_
  102.9 2.5 %collective-permute-start.49 = (f32[2,16,512]{2,1,0:T(8,128)S(1)}, f32[2,16,512]{2,1,0:T(8,128)S(1)}, u32[]{:S(2)}, u32[]{:S(2)}) collective-permute-start(f32[2,16,512]{2,1,0:T(8,128)S(1)} %get-tuple-element.85), channel_id=1, source_target_pairs={{0,24},{4,28},{8,16},{12,20},{16,8},{20,12},{24,0},{28,4},{1,25},{... | collective-permute-start | bytes 196616 | tf_op jit(solution)/shard_map/ppermute | solution.py:83
  106.4 1.0 shard_map.119
  107.4 0.7 collective-permute-done.49.refs_1_
  108.1 1.5 %collective-permute-done.50.refs_2_ = f32[2,16,512]{2,1,0:T(8,128)S(1)} collective-permute-done((f32[2,16,512]{2,1,0:T(8,128)S(1)}, f32[2,16,512]{2,1,0:T(8,128)S(1)}, u32[]{:S(2)}, u32[]{:S(2)}) %collective-permute-start.50) | collective-permute-done | bytes 65568 | tf_op jit(solution)/shard_map/ppermute | solution.py:83
  110.6 0.8 collective-permute-start.52
  111.3 3.0 %collective-permute-start.53 = (f32[16,1024]{1,0:T(8,128)S(1)}, f32[16,1024]{1,0:T(8,128)S(1)}, u32[]{:S(2)}, u32[]{:S(2)}) collective-permute-start(f32[16,1024]{1,0:T(8,128)S(1)} %get-tuple-element.89.refs_2_.refs_0_), channel_id=1, source_target_pairs={{0,3},{1,2},{2,1},{3,0},{4,7},{5,6},{6,5},{7,4},{8,11},{9,10},{10,... | collective-permute-start | bytes 196616 | tf_op jit(solution)/shard_map/ppermute | solution.py:33
  114.8 2.8 %collective-permute-done.52.refs_1_ = f32[16,1024]{1,0:T(8,128)S(1)} collective-permute-done((f32[16,1024]{1,0:T(8,128)S(1)}, f32[16,1024]{1,0:T(8,128)S(1)}, u32[]{:S(2)}, u32[]{:S(2)}) %collective-permute-start.52) | collective-permute-done | bytes 65568 | tf_op jit(solution)/shard_map/ppermute | solution.py:33
  117.6 1.0 collective-permute-done.54.refs_3_
  119.1 3.0 %collective-permute-start.56 = (f32[16,512]{1,0:T(8,128)S(1)}, f32[16,512]{1,0:T(8,128)S(1)}, u32[]{:S(2)}, u32[]{:S(2)}) collective-permute-start(f32[16,512]{1,0:T(8,128)S(1)} %get-tuple-element.98), channel_id=1, source_target_pairs={{0,3},{1,2},{2,1},{3,0},{4,7},{5,6},{6,5},{7,4},{8,11},{9,10},{10,... | collective-permute-start | bytes 98312 | tf_op jit(solution)/shard_map/ppermute | solution.py:33
  122.5 1.7 %collective-permute-done.55.refs_2_ = f32[16,512]{1,0:T(8,128)S(1)} collective-permute-done((f32[16,512]{1,0:T(8,128)S(1)}, f32[16,512]{1,0:T(8,128)S(1)}, u32[]{:S(2)}, u32[]{:S(2)}) %collective-permute-start.55) | collective-permute-done | bytes 32800 | tf_op jit(solution)/shard_map/ppermute | solution.py:33
  124.2 0.7 collective-permute-done.56.refs_3_
  124.8 1.1 collective-permute-done.57.refs_4_
  126.3 0.8 collective-permute-start.58
  127.1 2.1 %collective-permute-start.59 = (f32[16,256]{1,0:T(8,128)S(1)}, f32[16,256]{1,0:T(8,128)S(1)}, u32[]{:S(2)}, u32[]{:S(2)}) collective-permute-start(f32[16,256]{1,0:T(8,128)S(1)} %shard_map.124.refs_0_), channel_id=1, source_target_pairs={{0,3},{1,2},{2,1},{3,0},{4,7},{5,6},{6,5},{7,4},{8,11},{9,10},{10,... | collective-permute-start | bytes 49160 | tf_op jit(solution)/shard_map/ppermute | solution.py:33
  129.9 1.3 collective-permute-done.58.refs_1_
  131.2 1.5 %collective-permute-done.59.refs_2_ = f32[16,256]{1,0:T(8,128)S(1)} collective-permute-done((f32[16,256]{1,0:T(8,128)S(1)}, f32[16,256]{1,0:T(8,128)S(1)}, u32[]{:S(2)}, u32[]{:S(2)}) %collective-permute-start.59) | collective-permute-done | bytes 16416 | tf_op jit(solution)/shard_map/ppermute | solution.py:33
  133.0 1.0 shard_map.125
  (162 shorter events, 14.3 us)
Async XLA Ops:
  1.7 24.6 %copy-start.3 = (f32[1,4,256,128]{3,2,1,0:T(8,128)S(1)}, f32[1,4,256,128]{3,2,1,0:T(8,128)}, u32[]{:S(2)}) copy-start(f32[1,4,256,128]{3,2,1,0:T(8,128)} %rhs_ref.3) | copy-start | bytes 1572868
  1.9 10.1 %collective-permute-start = (f32[64,256]{1,0:T(8,128)S(1)}, f32[64,256]{1,0:T(8,128)S(1)}, u32[]{:S(2)}, u32[]{:S(2)}) collective-permute-start(f32[64,256]{1,0:T(8,128)S(1)} %get-tuple-element.52.refs_0_), channel_id=1, source_target_pairs={{0,1},{1,0},{2,3},{3,2},{4,5},{5,4},{6,7},{7,6},{8,9},{9,8},{10,11... | collective-permute-start | bytes 196616 | tf_op jit(solution)/shard_map/ppermute | solution.py:33
  5.0 9.1 %collective-permute-start.1 = (f32[64,256]{1,0:T(8,128)S(1)}, f32[64,256]{1,0:T(8,128)S(1)}, u32[]{:S(2)}, u32[]{:S(2)}) collective-permute-start(f32[64,256]{1,0:T(8,128)S(1)} %get-tuple-element.52.refs_0_), channel_id=1, source_target_pairs={{0,2},{1,3},{2,0},{3,1},{4,6},{5,7},{6,4},{7,5},{8,10},{9,11},{10,... | collective-permute-start | bytes 196616 | tf_op jit(solution)/shard_map/ppermute | solution.py:33
  7.6 6.6 %collective-permute-start.2 = (f32[64,256]{1,0:T(8,128)S(1)}, f32[64,256]{1,0:T(8,128)S(1)}, u32[]{:S(2)}, u32[]{:S(2)}) collective-permute-start(f32[64,256]{1,0:T(8,128)S(1)} %get-tuple-element.52.refs_0_), channel_id=1, source_target_pairs={{0,3},{1,2},{2,1},{3,0},{4,7},{5,6},{6,5},{7,4},{8,11},{9,10},{10,... | collective-permute-start | bytes 196616 | tf_op jit(solution)/shard_map/ppermute | solution.py:33
  7.6 13.6 %collective-permute-start.3 = (f32[64,256]{1,0:T(8,128)S(1)}, f32[64,256]{1,0:T(8,128)S(1)}, u32[]{:S(2)}, u32[]{:S(2)}) collective-permute-start(f32[64,256]{1,0:T(8,128)S(1)} %get-tuple-element.53.refs_0_), channel_id=1, source_target_pairs={{0,1},{1,0},{2,3},{3,2},{4,5},{5,4},{6,7},{7,6},{8,9},{9,8},{10,11... | collective-permute-start | bytes 196616 | tf_op jit(solution)/shard_map/ppermute | solution.py:33
  8.5 12.7 %collective-permute-start.4 = (f32[64,256]{1,0:T(8,128)S(1)}, f32[64,256]{1,0:T(8,128)S(1)}, u32[]{:S(2)}, u32[]{:S(2)}) collective-permute-start(f32[64,256]{1,0:T(8,128)S(1)} %get-tuple-element.53.refs_0_), channel_id=1, source_target_pairs={{0,2},{1,3},{2,0},{3,1},{4,6},{5,7},{6,4},{7,5},{8,10},{9,11},{10,... | collective-permute-start | bytes 196616 | tf_op jit(solution)/shard_map/ppermute | solution.py:33
  12.0 9.2 %collective-permute-start.5 = (f32[64,256]{1,0:T(8,128)S(1)}, f32[64,256]{1,0:T(8,128)S(1)}, u32[]{:S(2)}, u32[]{:S(2)}) collective-permute-start(f32[64,256]{1,0:T(8,128)S(1)} %get-tuple-element.53.refs_0_), channel_id=1, source_target_pairs={{0,3},{1,2},{2,1},{3,0},{4,7},{5,6},{6,5},{7,4},{8,11},{9,10},{10,... | collective-permute-start | bytes 196616 | tf_op jit(solution)/shard_map/ppermute | solution.py:33
  14.6 11.7 %collective-permute-start.6 = (f32[64,256]{1,0:T(8,128)S(1)}, f32[64,256]{1,0:T(8,128)S(1)}, u32[]{:S(2)}, u32[]{:S(2)}) collective-permute-start(f32[64,256]{1,0:T(8,128)S(1)} %shard_map.114.refs_0_), channel_id=1, source_target_pairs={{0,1},{1,0},{2,3},{3,2},{4,5},{5,4},{6,7},{7,6},{8,9},{9,8},{10,11... | collective-permute-start | bytes 196616 | tf_op jit(solution)/shard_map/ppermute | solution.py:33
  17.7 7.9 %collective-permute-start.7 = (f32[64,256]{1,0:T(8,128)S(1)}, f32[64,256]{1,0:T(8,128)S(1)}, u32[]{:S(2)}, u32[]{:S(2)}) collective-permute-start(f32[64,256]{1,0:T(8,128)S(1)} %shard_map.114.refs_0_), channel_id=1, source_target_pairs={{0,3},{1,2},{2,1},{3,0},{4,7},{5,6},{6,5},{7,4},{8,11},{9,10},{10,... | collective-permute-start | bytes 196616 | tf_op jit(solution)/shard_map/ppermute | solution.py:33
  21.2 7.0 %collective-permute-start.8 = (f32[64,256]{1,0:T(8,128)S(1)}, f32[64,256]{1,0:T(8,128)S(1)}, u32[]{:S(2)}, u32[]{:S(2)}) collective-permute-start(f32[64,256]{1,0:T(8,128)S(1)} %shard_map.114.refs_0_), channel_id=1, source_target_pairs={{0,2},{1,3},{2,0},{3,1},{4,6},{5,7},{6,4},{7,5},{8,10},{9,11},{10,... | collective-permute-start | bytes 196616 | tf_op jit(solution)/shard_map/ppermute | solution.py:33
  21.7 9.7 %collective-permute-start.9 = (f32[64,256]{1,0:T(8,128)S(1)}, f32[64,256]{1,0:T(8,128)S(1)}, u32[]{:S(2)}, u32[]{:S(2)}) collective-permute-start(f32[64,256]{1,0:T(8,128)S(1)} %shard_map.115.refs_1_), channel_id=1, source_target_pairs={{0,3},{1,2},{2,1},{3,0},{4,7},{5,6},{6,5},{7,4},{8,11},{9,10},{10,... | collective-permute-start | bytes 196616 | tf_op jit(solution)/shard_map/ppermute | solution.py:33
  23.5 9.9 %collective-permute-start.13 = (f32[64,256]{1,0:T(8,128)S(1)}, f32[64,256]{1,0:T(8,128)S(1)}, u32[]{:S(2)}, u32[]{:S(2)}) collective-permute-start(f32[64,256]{1,0:T(8,128)S(1)} %shard_map.115.refs_1_), channel_id=1, source_target_pairs={{0,2},{1,3},{2,0},{3,1},{4,6},{5,7},{6,4},{7,5},{8,10},{9,11},{10,... | collective-permute-start | bytes 196616 | tf_op jit(solution)/shard_map/ppermute | solution.py:33
  25.6 7.8 %collective-permute-start.12 = (f32[64,256]{1,0:T(8,128)S(1)}, f32[64,256]{1,0:T(8,128)S(1)}, u32[]{:S(2)}, u32[]{:S(2)}) collective-permute-start(f32[64,256]{1,0:T(8,128)S(1)} %shard_map.115.refs_1_), channel_id=1, source_target_pairs={{0,1},{1,0},{2,3},{3,2},{4,5},{5,4},{6,7},{7,6},{8,9},{9,8},{10,11... | collective-permute-start | bytes 196616 | tf_op jit(solution)/shard_map/ppermute | solution.py:33
  28.9 7.7 %collective-permute-start.11 = (f32[64,256]{1,0:T(8,128)S(1)}, f32[64,256]{1,0:T(8,128)S(1)}, u32[]{:S(2)}, u32[]{:S(2)}) collective-permute-start(f32[64,256]{1,0:T(8,128)S(1)} %get-tuple-element.56), channel_id=1, source_target_pairs={{0,3},{1,2},{2,1},{3,0},{4,7},{5,6},{6,5},{7,4},{8,11},{9,10},{10,... | collective-permute-start | bytes 196616 | tf_op jit(solution)/shard_map/ppermute | solution.py:33
  31.4 7.3 %collective-permute-start.14 = (f32[64,256]{1,0:T(8,128)S(1)}, f32[64,256]{1,0:T(8,128)S(1)}, u32[]{:S(2)}, u32[]{:S(2)}) collective-permute-start(f32[64,256]{1,0:T(8,128)S(1)} %get-tuple-element.56), channel_id=1, source_target_pairs={{0,2},{1,3},{2,0},{3,1},{4,6},{5,7},{6,4},{7,5},{8,10},{9,11},{10,... | collective-permute-start | bytes 196616 | tf_op jit(solution)/shard_map/ppermute | solution.py:33
  31.4 7.1 %collective-permute-start.10 = (f32[64,256]{1,0:T(8,128)S(1)}, f32[64,256]{1,0:T(8,128)S(1)}, u32[]{:S(2)}, u32[]{:S(2)}) collective-permute-start(f32[64,256]{1,0:T(8,128)S(1)} %get-tuple-element.56), channel_id=1, source_target_pairs={{0,1},{1,0},{2,3},{3,2},{4,5},{5,4},{6,7},{7,6},{8,9},{9,8},{10,11... | collective-permute-start | bytes 196616 | tf_op jit(solution)/shard_map/ppermute | solution.py:33
  34.1 7.9 %collective-permute-start.16 = (f32[64,256]{1,0:T(8,128)S(1)}, f32[64,256]{1,0:T(8,128)S(1)}, u32[]{:S(2)}, u32[]{:S(2)}) collective-permute-start(f32[64,256]{1,0:T(8,128)S(1)} %get-tuple-element.59), channel_id=1, source_target_pairs={{0,3},{1,2},{2,1},{3,0},{4,7},{5,6},{6,5},{7,4},{8,11},{9,10},{10,... | collective-permute-start | bytes 196616 | tf_op jit(solution)/shard_map/ppermute | solution.py:33
  36.6 7.8 %collective-permute-start.17 = (f32[64,256]{1,0:T(8,128)S(1)}, f32[64,256]{1,0:T(8,128)S(1)}, u32[]{:S(2)}, u32[]{:S(2)}) collective-permute-start(f32[64,256]{1,0:T(8,128)S(1)} %get-tuple-element.59), channel_id=1, source_target_pairs={{0,2},{1,3},{2,0},{3,1},{4,6},{5,7},{6,4},{7,5},{8,10},{9,11},{10,... | collective-permute-start | bytes 196616 | tf_op jit(solution)/shard_map/ppermute | solution.py:33
  36.6 7.3 %collective-permute-start.15 = (f32[64,256]{1,0:T(8,128)S(1)}, f32[64,256]{1,0:T(8,128)S(1)}, u32[]{:S(2)}, u32[]{:S(2)}) collective-permute-start(f32[64,256]{1,0:T(8,128)S(1)} %get-tuple-element.59), channel_id=1, source_target_pairs={{0,1},{1,0},{2,3},{3,2},{4,5},{5,4},{6,7},{7,6},{8,9},{9,8},{10,11... | collective-permute-start | bytes 196616 | tf_op jit(solution)/shard_map/ppermute | solution.py:33
  39.4 8.1 %collective-permute-start.19 = (f32[64,256]{1,0:T(8,128)S(1)}, f32[64,256]{1,0:T(8,128)S(1)}, u32[]{:S(2)}, u32[]{:S(2)}) collective-permute-start(f32[64,256]{1,0:T(8,128)S(1)} %get-tuple-element.61.refs_2_), channel_id=1, source_target_pairs={{0,3},{1,2},{2,1},{3,0},{4,7},{5,6},{6,5},{7,4},{8,11},{9,10},{10,... | collective-permute-start | bytes 196616 | tf_op jit(solution)/shard_map/ppermute | solution.py:33
  41.9 8.0 %collective-permute-start.20 = (f32[64,256]{1,0:T(8,128)S(1)}, f32[64,256]{1,0:T(8,128)S(1)}, u32[]{:S(2)}, u32[]{:S(2)}) collective-permute-start(f32[64,256]{1,0:T(8,128)S(1)} %get-tuple-element.61.refs_2_), channel_id=1, source_target_pairs={{0,2},{1,3},{2,0},{3,1},{4,6},{5,7},{6,4},{7,5},{8,10},{9,11},{10,... | collective-permute-start | bytes 196616 | tf_op jit(solution)/shard_map/ppermute | solution.py:33
  41.9 7.5 %collective-permute-start.18 = (f32[64,256]{1,0:T(8,128)S(1)}, f32[64,256]{1,0:T(8,128)S(1)}, u32[]{:S(2)}, u32[]{:S(2)}) collective-permute-start(f32[64,256]{1,0:T(8,128)S(1)} %get-tuple-element.61.refs_2_), channel_id=1, source_target_pairs={{0,1},{1,0},{2,3},{3,2},{4,5},{5,4},{6,7},{7,6},{8,9},{9,8},{10,11... | collective-permute-start | bytes 196616 | tf_op jit(solution)/shard_map/ppermute | solution.py:33
  45.0 8.2 %collective-permute-start.21 = (f32[64,256]{1,0:T(8,128)S(1)}, f32[64,256]{1,0:T(8,128)S(1)}, u32[]{:S(2)}, u32[]{:S(2)}) collective-permute-start(f32[64,256]{1,0:T(8,128)S(1)} %get-tuple-element.65.refs_3_), channel_id=1, source_target_pairs={{0,3},{1,2},{2,1},{3,0},{4,7},{5,6},{6,5},{7,4},{8,11},{9,10},{10,... | collective-permute-start | bytes 196616 | tf_op jit(solution)/shard_map/ppermute | solution.py:33
  47.5 8.0 %collective-permute-start.25 = (f32[64,256]{1,0:T(8,128)S(1)}, f32[64,256]{1,0:T(8,128)S(1)}, u32[]{:S(2)}, u32[]{:S(2)}) collective-permute-start(f32[64,256]{1,0:T(8,128)S(1)} %get-tuple-element.65.refs_3_), channel_id=1, source_target_pairs={{0,2},{1,3},{2,0},{3,1},{4,6},{5,7},{6,4},{7,5},{8,10},{9,11},{10,... | collective-permute-start | bytes 196616 | tf_op jit(solution)/shard_map/ppermute | solution.py:33
  47.6 7.5 %collective-permute-start.24 = (f32[64,256]{1,0:T(8,128)S(1)}, f32[64,256]{1,0:T(8,128)S(1)}, u32[]{:S(2)}, u32[]{:S(2)}) collective-permute-start(f32[64,256]{1,0:T(8,128)S(1)} %get-tuple-element.65.refs_3_), channel_id=1, source_target_pairs={{0,1},{1,0},{2,3},{3,2},{4,5},{5,4},{6,7},{7,6},{8,9},{9,8},{10,11... | collective-permute-start | bytes 196616 | tf_op jit(solution)/shard_map/ppermute | solution.py:33
  50.6 8.2 %collective-permute-start.23 = (f32[64,256]{1,0:T(8,128)S(1)}, f32[64,256]{1,0:T(8,128)S(1)}, u32[]{:S(2)}, u32[]{:S(2)}) collective-permute-start(f32[64,256]{1,0:T(8,128)S(1)} %get-tuple-element.64), channel_id=1, source_target_pairs={{0,3},{1,2},{2,1},{3,0},{4,7},{5,6},{6,5},{7,4},{8,11},{9,10},{10,... | collective-permute-start | bytes 196616 | tf_op jit(solution)/shard_map/ppermute | solution.py:33
  53.2 8.0 %collective-permute-start.26 = (f32[64,256]{1,0:T(8,128)S(1)}, f32[64,256]{1,0:T(8,128)S(1)}, u32[]{:S(2)}, u32[]{:S(2)}) collective-permute-start(f32[64,256]{1,0:T(8,128)S(1)} %get-tuple-element.64), channel_id=1, source_target_pairs={{0,2},{1,3},{2,0},{3,1},{4,6},{5,7},{6,4},{7,5},{8,10},{9,11},{10,... | collective-permute-start | bytes 196616 | tf_op jit(solution)/shard_map/ppermute | solution.py:33
  53.2 7.5 %collective-permute-start.22 = (f32[64,256]{1,0:T(8,128)S(1)}, f32[64,256]{1,0:T(8,128)S(1)}, u32[]{:S(2)}, u32[]{:S(2)}) collective-permute-start(f32[64,256]{1,0:T(8,128)S(1)} %get-tuple-element.64), channel_id=1, source_target_pairs={{0,1},{1,0},{2,3},{3,2},{4,5},{5,4},{6,7},{7,6},{8,9},{9,8},{10,11... | collective-permute-start | bytes 196616 | tf_op jit(solution)/shard_map/ppermute | solution.py:33
  56.3 8.2 %collective-permute-start.28 = (f32[64,256]{1,0:T(8,128)S(1)}, f32[64,256]{1,0:T(8,128)S(1)}, u32[]{:S(2)}, u32[]{:S(2)}) collective-permute-start(f32[64,256]{1,0:T(8,128)S(1)} %get-tuple-element.67), channel_id=1, source_target_pairs={{0,3},{1,2},{2,1},{3,0},{4,7},{5,6},{6,5},{7,4},{8,11},{9,10},{10,... | collective-permute-start | bytes 196616 | tf_op jit(solution)/shard_map/ppermute | solution.py:33
  58.8 8.0 %collective-permute-start.29 = (f32[64,256]{1,0:T(8,128)S(1)}, f32[64,256]{1,0:T(8,128)S(1)}, u32[]{:S(2)}, u32[]{:S(2)}) collective-permute-start(f32[64,256]{1,0:T(8,128)S(1)} %get-tuple-element.67), channel_id=1, source_target_pairs={{0,2},{1,3},{2,0},{3,1},{4,6},{5,7},{6,4},{7,5},{8,10},{9,11},{10,... | collective-permute-start | bytes 196616 | tf_op jit(solution)/shard_map/ppermute | solution.py:33
  58.8 7.5 %collective-permute-start.27 = (f32[64,256]{1,0:T(8,128)S(1)}, f32[64,256]{1,0:T(8,128)S(1)}, u32[]{:S(2)}, u32[]{:S(2)}) collective-permute-start(f32[64,256]{1,0:T(8,128)S(1)} %get-tuple-element.67), channel_id=1, source_target_pairs={{0,1},{1,0},{2,3},{3,2},{4,5},{5,4},{6,7},{7,6},{8,9},{9,8},{10,11... | collective-permute-start | bytes 196616 | tf_op jit(solution)/shard_map/ppermute | solution.py:33
  61.9 8.2 %collective-permute-start.31 = (f32[64,256]{1,0:T(8,128)S(1)}, f32[64,256]{1,0:T(8,128)S(1)}, u32[]{:S(2)}, u32[]{:S(2)}) collective-permute-start(f32[64,256]{1,0:T(8,128)S(1)} %get-tuple-element.69.refs_4_), channel_id=1, source_target_pairs={{0,3},{1,2},{2,1},{3,0},{4,7},{5,6},{6,5},{7,4},{8,11},{9,10},{10,... | collective-permute-start | bytes 196616 | tf_op jit(solution)/shard_map/ppermute | solution.py:33
  64.4 8.0 %collective-permute-start.32 = (f32[64,256]{1,0:T(8,128)S(1)}, f32[64,256]{1,0:T(8,128)S(1)}, u32[]{:S(2)}, u32[]{:S(2)}) collective-permute-start(f32[64,256]{1,0:T(8,128)S(1)} %get-tuple-element.69.refs_4_), channel_id=1, source_target_pairs={{0,2},{1,3},{2,0},{3,1},{4,6},{5,7},{6,4},{7,5},{8,10},{9,11},{10,... | collective-permute-start | bytes 196616 | tf_op jit(solution)/shard_map/ppermute | solution.py:33
  64.4 7.5 %collective-permute-start.30 = (f32[64,256]{1,0:T(8,128)S(1)}, f32[64,256]{1,0:T(8,128)S(1)}, u32[]{:S(2)}, u32[]{:S(2)}) collective-permute-start(f32[64,256]{1,0:T(8,128)S(1)} %get-tuple-element.69.refs_4_), channel_id=1, source_target_pairs={{0,1},{1,0},{2,3},{3,2},{4,5},{5,4},{6,7},{7,6},{8,9},{9,8},{10,11... | collective-permute-start | bytes 196616 | tf_op jit(solution)/shard_map/ppermute | solution.py:33
  67.5 8.2 %collective-permute-start.33 = (f32[64,256]{1,0:T(8,128)S(1)}, f32[64,256]{1,0:T(8,128)S(1)}, u32[]{:S(2)}, u32[]{:S(2)}) collective-permute-start(f32[64,256]{1,0:T(8,128)S(1)} %get-tuple-element.73.refs_5_), channel_id=1, source_target_pairs={{0,3},{1,2},{2,1},{3,0},{4,7},{5,6},{6,5},{7,4},{8,11},{9,10},{10,... | collective-permute-start | bytes 196616 | tf_op jit(solution)/shard_map/ppermute | solution.py:33
  70.0 8.0 %collective-permute-start.37 = (f32[64,256]{1,0:T(8,128)S(1)}, f32[64,256]{1,0:T(8,128)S(1)}, u32[]{:S(2)}, u32[]{:S(2)}) collective-permute-start(f32[64,256]{1,0:T(8,128)S(1)} %get-tuple-element.73.refs_5_), channel_id=1, source_target_pairs={{0,2},{1,3},{2,0},{3,1},{4,6},{5,7},{6,4},{7,5},{8,10},{9,11},{10,... | collective-permute-start | bytes 196616 | tf_op jit(solution)/shard_map/ppermute | solution.py:33
  70.0 7.5 %collective-permute-start.36 = (f32[64,256]{1,0:T(8,128)S(1)}, f32[64,256]{1,0:T(8,128)S(1)}, u32[]{:S(2)}, u32[]{:S(2)}) collective-permute-start(f32[64,256]{1,0:T(8,128)S(1)} %get-tuple-element.73.refs_5_), channel_id=1, source_target_pairs={{0,1},{1,0},{2,3},{3,2},{4,5},{5,4},{6,7},{7,6},{8,9},{9,8},{10,11... | collective-permute-start | bytes 196616 | tf_op jit(solution)/shard_map/ppermute | solution.py:33
  73.1 8.2 %collective-permute-start.35 = (f32[64,256]{1,0:T(8,128)S(1)}, f32[64,256]{1,0:T(8,128)S(1)}, u32[]{:S(2)}, u32[]{:S(2)}) collective-permute-start(f32[64,256]{1,0:T(8,128)S(1)} %get-tuple-element.72), channel_id=1, source_target_pairs={{0,3},{1,2},{2,1},{3,0},{4,7},{5,6},{6,5},{7,4},{8,11},{9,10},{10,... | collective-permute-start | bytes 196616 | tf_op jit(solution)/shard_map/ppermute | solution.py:33
  75.6 8.0 %collective-permute-start.38 = (f32[64,256]{1,0:T(8,128)S(1)}, f32[64,256]{1,0:T(8,128)S(1)}, u32[]{:S(2)}, u32[]{:S(2)}) collective-permute-start(f32[64,256]{1,0:T(8,128)S(1)} %get-tuple-element.72), channel_id=1, source_target_pairs={{0,2},{1,3},{2,0},{3,1},{4,6},{5,7},{6,4},{7,5},{8,10},{9,11},{10,... | collective-permute-start | bytes 196616 | tf_op jit(solution)/shard_map/ppermute | solution.py:33
  75.6 7.6 %collective-permute-start.34 = (f32[64,256]{1,0:T(8,128)S(1)}, f32[64,256]{1,0:T(8,128)S(1)}, u32[]{:S(2)}, u32[]{:S(2)}) collective-permute-start(f32[64,256]{1,0:T(8,128)S(1)} %get-tuple-element.72), channel_id=1, source_target_pairs={{0,1},{1,0},{2,3},{3,2},{4,5},{5,4},{6,7},{7,6},{8,9},{9,8},{10,11... | collective-permute-start | bytes 196616 | tf_op jit(solution)/shard_map/ppermute | solution.py:33
  78.1 20.8 %copy-start = (f32[1,1,3,128,1024]{4,3,2,1,0:T(8,128)S(1)}, f32[1,1,3,128,1024]{4,3,2,1,0:T(8,128)}, u32[]{:S(2)}) copy-start(f32[1,1,3,128,1024]{4,3,2,1,0:T(8,128)} %param.13) | copy-start | bytes 4718596
  78.1 20.8 %copy-start.6 = (s32[1,1,3]{2,1,0:T(1,128)S(1)}, s32[1,1,3]{2,1,0:T(1,128)}, u32[]{:S(2)}) copy-start(s32[1,1,3]{2,1,0:T(1,128)} %refs_6_.1) | copy-start | bytes 40
  78.7 8.1 %collective-permute-start.40 = (f32[64,256]{1,0:T(8,128)S(1)}, f32[64,256]{1,0:T(8,128)S(1)}, u32[]{:S(2)}, u32[]{:S(2)}) collective-permute-start(f32[64,256]{1,0:T(8,128)S(1)} %get-tuple-element.75), channel_id=1, source_target_pairs={{0,3},{1,2},{2,1},{3,0},{4,7},{5,6},{6,5},{7,4},{8,11},{9,10},{10,... | collective-permute-start | bytes 196616 | tf_op jit(solution)/shard_map/ppermute | solution.py:33
  81.3 10.8 %collective-permute-start.41 = (f32[64,256]{1,0:T(8,128)S(1)}, f32[64,256]{1,0:T(8,128)S(1)}, u32[]{:S(2)}, u32[]{:S(2)}) collective-permute-start(f32[64,256]{1,0:T(8,128)S(1)} %get-tuple-element.75), channel_id=1, source_target_pairs={{0,2},{1,3},{2,0},{3,1},{4,6},{5,7},{6,4},{7,5},{8,10},{9,11},{10,... | collective-permute-start | bytes 196616 | tf_op jit(solution)/shard_map/ppermute | solution.py:33
  81.3 7.5 %collective-permute-start.39 = (f32[64,256]{1,0:T(8,128)S(1)}, f32[64,256]{1,0:T(8,128)S(1)}, u32[]{:S(2)}, u32[]{:S(2)}) collective-permute-start(f32[64,256]{1,0:T(8,128)S(1)} %get-tuple-element.75), channel_id=1, source_target_pairs={{0,1},{1,0},{2,3},{3,2},{4,5},{5,4},{6,7},{7,6},{8,9},{9,8},{10,11... | collective-permute-start | bytes 196616 | tf_op jit(solution)/shard_map/ppermute | solution.py:33
  84.3 8.6 %collective-permute-start.43 = (f32[64,256]{1,0:T(8,128)S(1)}, f32[64,256]{1,0:T(8,128)S(1)}, u32[]{:S(2)}, u32[]{:S(2)}) collective-permute-start(f32[64,256]{1,0:T(8,128)S(1)} %get-tuple-element.77.refs_6_), channel_id=1, source_target_pairs={{0,3},{1,2},{2,1},{3,0},{4,7},{5,6},{6,5},{7,4},{8,11},{9,10},{10,... | collective-permute-start | bytes 196616 | tf_op jit(solution)/shard_map/ppermute | solution.py:33
  86.9 10.4 %collective-permute-start.44 = (f32[64,256]{1,0:T(8,128)S(1)}, f32[64,256]{1,0:T(8,128)S(1)}, u32[]{:S(2)}, u32[]{:S(2)}) collective-permute-start(f32[64,256]{1,0:T(8,128)S(1)} %get-tuple-element.77.refs_6_), channel_id=1, source_target_pairs={{0,2},{1,3},{2,0},{3,1},{4,6},{5,7},{6,4},{7,5},{8,10},{9,11},{10,... | collective-permute-start | bytes 196616 | tf_op jit(solution)/shard_map/ppermute | solution.py:33
  86.9 10.3 %collective-permute-start.42 = (f32[64,256]{1,0:T(8,128)S(1)}, f32[64,256]{1,0:T(8,128)S(1)}, u32[]{:S(2)}, u32[]{:S(2)}) collective-permute-start(f32[64,256]{1,0:T(8,128)S(1)} %get-tuple-element.77.refs_6_), channel_id=1, source_target_pairs={{0,1},{1,0},{2,3},{3,2},{4,5},{5,4},{6,7},{7,6},{8,9},{9,8},{10,11... | collective-permute-start | bytes 196616 | tf_op jit(solution)/shard_map/ppermute | solution.py:33
  92.8 6.1 %collective-permute-start.46 = (f32[64,256]{1,0:T(8,128)S(1)}, f32[64,256]{1,0:T(8,128)S(1)}, u32[]{:S(2)}, u32[]{:S(2)}) collective-permute-start(f32[64,256]{1,0:T(8,128)S(1)} %get-tuple-element.79.refs_7_), channel_id=1, source_target_pairs={{0,3},{1,2},{2,1},{3,0},{4,7},{5,6},{6,5},{7,4},{8,11},{9,10},{10,... | collective-permute-start | bytes 196616 | tf_op jit(solution)/shard_map/ppermute | solution.py:33
  92.8 7.3 %collective-permute-start.47 = (f32[64,256]{1,0:T(8,128)S(1)}, f32[64,256]{1,0:T(8,128)S(1)}, u32[]{:S(2)}, u32[]{:S(2)}) collective-permute-start(f32[64,256]{1,0:T(8,128)S(1)} %get-tuple-element.79.refs_7_), channel_id=1, source_target_pairs={{0,2},{1,3},{2,0},{3,1},{4,6},{5,7},{6,4},{7,5},{8,10},{9,11},{10,... | collective-permute-start | bytes 196616 | tf_op jit(solution)/shard_map/ppermute | solution.py:33
  92.9 7.2 %collective-permute-start.45 = (f32[64,256]{1,0:T(8,128)S(1)}, f32[64,256]{1,0:T(8,128)S(1)}, u32[]{:S(2)}, u32[]{:S(2)}) collective-permute-start(f32[64,256]{1,0:T(8,128)S(1)} %get-tuple-element.79.refs_7_), channel_id=1, source_target_pairs={{0,1},{1,0},{2,3},{3,2},{4,5},{5,4},{6,7},{7,6},{8,9},{9,8},{10,11... | collective-permute-start | bytes 196616 | tf_op jit(solution)/shard_map/ppermute | solution.py:33
  101.4 1.4 %collective-permute-start.48 = (f32[4,16,512]{2,1,0:T(8,128)S(1)}, f32[4,16,512]{2,1,0:T(8,128)S(1)}, u32[]{:S(2)}, u32[]{:S(2)}) collective-permute-start(f32[4,16,512]{2,1,0:T(8,128)S(1)} %get-tuple-element.83), channel_id=1, source_target_pairs={{0,4},{4,0},{8,12},{12,8},{16,20},{20,16},{24,28},{28,24},{1,5},{5... | collective-permute-start | bytes 393224 | tf_op jit(solution)/shard_map/ppermute | solution.py:283
  102.9 5.3 %collective-permute-start.49 = (f32[2,16,512]{2,1,0:T(8,128)S(1)}, f32[2,16,512]{2,1,0:T(8,128)S(1)}, u32[]{:S(2)}, u32[]{:S(2)}) collective-permute-start(f32[2,16,512]{2,1,0:T(8,128)S(1)} %get-tuple-element.85), channel_id=1, source_target_pairs={{0,24},{4,28},{8,16},{12,20},{16,8},{20,12},{24,0},{28,4},{1,25},{... | collective-permute-start | bytes 196616 | tf_op jit(solution)/shard_map/ppermute | solution.py:83
  105.4 4.3 %collective-permute-start.50 = (f32[2,16,512]{2,1,0:T(8,128)S(1)}, f32[2,16,512]{2,1,0:T(8,128)S(1)}, u32[]{:S(2)}, u32[]{:S(2)}) collective-permute-start(f32[2,16,512]{2,1,0:T(8,128)S(1)} %get-tuple-element.86), channel_id=1, source_target_pairs={{0,16},{4,20},{8,24},{12,28},{16,0},{20,4},{24,8},{28,12},{1,17},{... | collective-permute-start | bytes 196616 | tf_op jit(solution)/shard_map/ppermute | solution.py:83
  105.9 4.3 %collective-permute-start.51 = (f32[2,16,512]{2,1,0:T(8,128)S(1)}, f32[2,16,512]{2,1,0:T(8,128)S(1)}, u32[]{:S(2)}, u32[]{:S(2)}) collective-permute-start(f32[2,16,512]{2,1,0:T(8,128)S(1)} %get-tuple-element.87), channel_id=1, source_target_pairs={{0,8},{4,12},{8,0},{12,4},{16,24},{20,28},{24,16},{28,20},{1,9},{5... | collective-permute-start | bytes 196616 | tf_op jit(solution)/shard_map/ppermute | solution.py:83
  110.6 7.0 %collective-permute-start.52 = (f32[16,1024]{1,0:T(8,128)S(1)}, f32[16,1024]{1,0:T(8,128)S(1)}, u32[]{:S(2)}, u32[]{:S(2)}) collective-permute-start(f32[16,1024]{1,0:T(8,128)S(1)} %get-tuple-element.89.refs_2_.refs_0_), channel_id=1, source_target_pairs={{0,2},{1,3},{2,0},{3,1},{4,6},{5,7},{6,4},{7,5},{8,10},{9,11},{10,... | collective-permute-start | bytes 196616 | tf_op jit(solution)/shard_map/ppermute | solution.py:33
  111.3 6.2 %collective-permute-start.53 = (f32[16,1024]{1,0:T(8,128)S(1)}, f32[16,1024]{1,0:T(8,128)S(1)}, u32[]{:S(2)}, u32[]{:S(2)}) collective-permute-start(f32[16,1024]{1,0:T(8,128)S(1)} %get-tuple-element.89.refs_2_.refs_0_), channel_id=1, source_target_pairs={{0,3},{1,2},{2,1},{3,0},{4,7},{5,6},{6,5},{7,4},{8,11},{9,10},{10,... | collective-permute-start | bytes 196616 | tf_op jit(solution)/shard_map/ppermute | solution.py:33
  114.3 4.3 %collective-permute-start.54 = (f32[16,1024]{1,0:T(8,128)S(1)}, f32[16,1024]{1,0:T(8,128)S(1)}, u32[]{:S(2)}, u32[]{:S(2)}) collective-permute-start(f32[16,1024]{1,0:T(8,128)S(1)} %get-tuple-element.89.refs_2_.refs_0_), channel_id=1, source_target_pairs={{0,1},{1,0},{2,3},{3,2},{4,5},{5,4},{6,7},{7,6},{8,9},{9,8},{10,11... | collective-permute-start | bytes 196616 | tf_op jit(solution)/shard_map/ppermute | solution.py:33
  119.0 5.2 %collective-permute-start.55 = (f32[16,512]{1,0:T(8,128)S(1)}, f32[16,512]{1,0:T(8,128)S(1)}, u32[]{:S(2)}, u32[]{:S(2)}) collective-permute-start(f32[16,512]{1,0:T(8,128)S(1)} %get-tuple-element.97), channel_id=1, source_target_pairs={{0,2},{1,3},{2,0},{3,1},{4,6},{5,7},{6,4},{7,5},{8,10},{9,11},{10,... | collective-permute-start | bytes 98312 | tf_op jit(solution)/shard_map/ppermute | solution.py:33
  119.1 5.8 %collective-permute-start.56 = (f32[16,512]{1,0:T(8,128)S(1)}, f32[16,512]{1,0:T(8,128)S(1)}, u32[]{:S(2)}, u32[]{:S(2)}) collective-permute-start(f32[16,512]{1,0:T(8,128)S(1)} %get-tuple-element.98), channel_id=1, source_target_pairs={{0,3},{1,2},{2,1},{3,0},{4,7},{5,6},{6,5},{7,4},{8,11},{9,10},{10,... | collective-permute-start | bytes 98312 | tf_op jit(solution)/shard_map/ppermute | solution.py:33
  122.1 3.9 %collective-permute-start.57 = (f32[16,512]{1,0:T(8,128)S(1)}, f32[16,512]{1,0:T(8,128)S(1)}, u32[]{:S(2)}, u32[]{:S(2)}) collective-permute-start(f32[16,512]{1,0:T(8,128)S(1)} %get-tuple-element.99), channel_id=1, source_target_pairs={{0,1},{1,0},{2,3},{3,2},{4,5},{5,4},{6,7},{7,6},{8,9},{9,8},{10,11... | collective-permute-start | bytes 98312 | tf_op jit(solution)/shard_map/ppermute | solution.py:33
  126.3 4.8 %collective-permute-start.58 = (f32[16,256]{1,0:T(8,128)S(1)}, f32[16,256]{1,0:T(8,128)S(1)}, u32[]{:S(2)}, u32[]{:S(2)}) collective-permute-start(f32[16,256]{1,0:T(8,128)S(1)} %shard_map.124.refs_0_), channel_id=1, source_target_pairs={{0,2},{1,3},{2,0},{3,1},{4,6},{5,7},{6,4},{7,5},{8,10},{9,11},{10,... | collective-permute-start | bytes 49160 | tf_op jit(solution)/shard_map/ppermute | solution.py:33
  127.1 5.5 %collective-permute-start.59 = (f32[16,256]{1,0:T(8,128)S(1)}, f32[16,256]{1,0:T(8,128)S(1)}, u32[]{:S(2)}, u32[]{:S(2)}) collective-permute-start(f32[16,256]{1,0:T(8,128)S(1)} %shard_map.124.refs_0_), channel_id=1, source_target_pairs={{0,3},{1,2},{2,1},{3,0},{4,7},{5,6},{6,5},{7,4},{8,11},{9,10},{10,... | collective-permute-start | bytes 49160 | tf_op jit(solution)/shard_map/ppermute | solution.py:33
  129.3 3.7 %collective-permute-start.60 = (f32[16,256]{1,0:T(8,128)S(1)}, f32[16,256]{1,0:T(8,128)S(1)}, u32[]{:S(2)}, u32[]{:S(2)}) collective-permute-start(f32[16,256]{1,0:T(8,128)S(1)} %shard_map.124.refs_0_), channel_id=1, source_target_pairs={{0,1},{1,0},{2,3},{3,2},{4,5},{5,4},{6,7},{7,6},{8,9},{9,8},{10,11... | collective-permute-start | bytes 49160 | tf_op jit(solution)/shard_map/ppermute | solution.py:33
  (7 other events, 86.4 us)

commit v24 on v22

--- a/solution.py
+++ b/solution.py
@@ -33,12 +33,14 @@
     return lax.ppermute(value, axis, pairs)
 
 
-def gather_rows(value, ties=(), far_first=False):
+def gather_rows(value, ties=(), swapped=False, far_first=False):
     members = lax.axis_size("grp")
     me = lax.axis_index("grp")
     rows = value.shape[1]
     pieces = [(me * rows, value)]
     distances = list(range(1, members))
+    if swapped:
+        distances[1:] = distances[:0:-1]
     if far_first:
         distances = distances[1:] + distances[:1]
     for distance in distances:
@@ -494,15 +496,16 @@
         for i in range(streams):
             turn_taken = step > 0 and last is not None
             ties = [(1, last[0][2][1])] if step * streams + i > streams else []
-            pieces = gather_rows(values[i], ties)
+            pieces = gather_rows(values[i], ties, i % 2 == 1 and step + 1 < 2 * supernodes)
             if step == 1 and i == 0:
                 later = turn(rhs_local, 1, supernodes, streams, pieces[1][1])
             if turn_taken:
                 offset, piece = pieces[2]
                 pieces[2] = (offset, lax.optimization_barrier((piece, last[1]))[0])
             if step == 0:
+                in_turn = pieces[:2] + pieces[:1:-1] if i % 2 else pieces
                 owned = apply_split(
-                    [p for _, p in pieces],
+                    [p for _, p in in_turn],
                     first_top,
                     first_rest,
                     0,

time: 134 us -> 137 us (1.022)
  waiting for transfers between devices: 22.9 us -> 30.8 us
  starting transfers between devices: 90.2 us -> 85.3 us
    ppermute x57, waiting for transfers between devices: 18.9 us -> 26.8 us  [send(): return lax.ppermute(value, axis, pairs)]
    ppermute x57, starting transfers between devices: 86.6 us -> 81.6 us  [send(): return lax.ppermute(value, axis, pairs)]
  transfers between devices with their start and end apart: 61 -> 61, of which waited for: 18 -> 24; matrix products, arithmetic and copies ran while one was open for 7% -> 7% of each run, Pallas kernels for 3% -> 3%
where the time goes in v24:
time: 137 us; the launch traced here: 136 us
  starting transfers between devices  85.3 us (62%)
  waiting for transfers between devices  30.8 us (22%)
  Pallas kernels  7.53 us (5%)
  matrix products  7.53 us (5%)
  between operations  2 us (1%)
  local copies, waits for them, and re-layouts  1.81 us (1%)
  other arithmetic  1.41 us (1%)
    ppermute x57, starting transfers between devices, send(): return lax.ppermute(value, axis, pairs)  81.6 us
    ppermute x57, waiting for transfers between devices, send(): return lax.ppermute(value, axis, pairs)  26.8 us
    dot_general x12, matrix products, contract_last(): lax.dot_general(left, right, (((left.ndim - 1,), (right.ndim - 1,)), ((),...  7.53 us
    pallas_call x13, Pallas kernels, local_kernel(): pl.pallas_call(body, out_shape=list(outs), in_specs=specs or [VMEM] * len...  7.53 us
    ppermute x3, starting transfers between devices, swap(): return lax.ppermute(value, axis, pairs)  3.55 us
  transfers between devices with their start and end apart: 61, of which 24 were waited for; matrix products, arithmetic and copies ran while one was open for 7% of the time, Pallas kernels for 3%

profile of v24, /device:TPU:0, one launch (start us, length us, event | category | flops | bytes accessed | tf_op | source)
XLA Modules:
  0.0 136.4 jit_solution(4003299806958042509)
XLA Ops:
  0.6 1.0 copy-done.2
  1.9 3.1 %collective-permute-start = (f32[64,256]{1,0:T(8,128)S(1)}, f32[64,256]{1,0:T(8,128)S(1)}, u32[]{:S(2)}, u32[]{:S(2)}) collective-permute-start(f32[64,256]{1,0:T(8,128)S(1)} %get-tuple-element.52.refs_0_), channel_id=1, source_target_pairs={{0,1},{1,0},{2,3},{3,2},{4,5},{5,4},{6,7},{7,6},{8,9},{9,8},{10,11... | collective-permute-start | bytes 196616 | tf_op jit(solution)/shard_map/ppermute | solution.py:33
  5.0 2.6 %collective-permute-start.1 = (f32[64,256]{1,0:T(8,128)S(1)}, f32[64,256]{1,0:T(8,128)S(1)}, u32[]{:S(2)}, u32[]{:S(2)}) collective-permute-start(f32[64,256]{1,0:T(8,128)S(1)} %get-tuple-element.52.refs_0_), channel_id=1, source_target_pairs={{0,2},{1,3},{2,0},{3,1},{4,6},{5,7},{6,4},{7,5},{8,10},{9,11},{10,... | collective-permute-start | bytes 196616 | tf_op jit(solution)/shard_map/ppermute | solution.py:33
  7.6 0.9 collective-permute-start.3
  8.5 3.5 %collective-permute-start.4 = (f32[64,256]{1,0:T(8,128)S(1)}, f32[64,256]{1,0:T(8,128)S(1)}, u32[]{:S(2)}, u32[]{:S(2)}) collective-permute-start(f32[64,256]{1,0:T(8,128)S(1)} %get-tuple-element.53.refs_0_), channel_id=1, source_target_pairs={{0,2},{1,3},{2,0},{3,1},{4,6},{5,7},{6,4},{7,5},{8,10},{9,11},{10,... | collective-permute-start | bytes 196616 | tf_op jit(solution)/shard_map/ppermute | solution.py:33
  12.0 1.4 %fusion = (bf16[1,256,1024]{2,1,0:T(8,128)(2,1)S(1)}, bf16[1,256,1024]{2,1,0:T(8,128)(2,1)S(1)}) fusion(f32[1,4,256,1024]{3,2,1,0:T(8,128)} %param.11), kind=kLoop, calls=%fused_computation.2 | loop fusion | flops 1048576 | bytes 2097152 | tf_op jit(solution)/shard_map/convert_element_type | solution.py:489
  14.6 3.0 %collective-permute-start.6 = (f32[64,256]{1,0:T(8,128)S(1)}, f32[64,256]{1,0:T(8,128)S(1)}, u32[]{:S(2)}, u32[]{:S(2)}) collective-permute-start(f32[64,256]{1,0:T(8,128)S(1)} %shard_map.114.refs_0_), channel_id=1, source_target_pairs={{0,1},{1,0},{2,3},{3,2},{4,5},{5,4},{6,7},{7,6},{8,9},{9,8},{10,11... | collective-permute-start | bytes 196616 | tf_op jit(solution)/shard_map/ppermute | solution.py:33
  17.7 2.1 %collective-permute-start.7 = (f32[64,256]{1,0:T(8,128)S(1)}, f32[64,256]{1,0:T(8,128)S(1)}, u32[]{:S(2)}, u32[]{:S(2)}) collective-permute-start(f32[64,256]{1,0:T(8,128)S(1)} %shard_map.114.refs_0_), channel_id=1, source_target_pairs={{0,2},{1,3},{2,0},{3,1},{4,6},{5,7},{6,4},{7,5},{8,10},{9,11},{10,... | collective-permute-start | bytes 196616 | tf_op jit(solution)/shard_map/ppermute | solution.py:33
  19.8 1.4 %collective-permute-start.8 = (f32[64,256]{1,0:T(8,128)S(1)}, f32[64,256]{1,0:T(8,128)S(1)}, u32[]{:S(2)}, u32[]{:S(2)}) collective-permute-start(f32[64,256]{1,0:T(8,128)S(1)} %shard_map.114.refs_0_), channel_id=1, source_target_pairs={{0,3},{1,2},{2,1},{3,0},{4,7},{5,6},{6,5},{7,4},{8,11},{9,10},{10,... | collective-permute-start | bytes 196616 | tf_op jit(solution)/shard_map/ppermute | solution.py:33
  21.7 2.5 %collective-permute-start.9 = (f32[64,256]{1,0:T(8,128)S(1)}, f32[64,256]{1,0:T(8,128)S(1)}, u32[]{:S(2)}, u32[]{:S(2)}) collective-permute-start(f32[64,256]{1,0:T(8,128)S(1)} %shard_map.115.refs_1_), channel_id=1, source_target_pairs={{0,3},{1,2},{2,1},{3,0},{4,7},{5,6},{6,5},{7,4},{8,11},{9,10},{10,... | collective-permute-start | bytes 196616 | tf_op jit(solution)/shard_map/ppermute | solution.py:33
  24.3 1.4 %collective-permute-done.7 = f32[64,256]{1,0:T(8,128)S(1)} collective-permute-done((f32[64,256]{1,0:T(8,128)S(1)}, f32[64,256]{1,0:T(8,128)S(1)}, u32[]{:S(2)}, u32[]{:S(2)}) %collective-permute-start.7) | collective-permute-done | bytes 65568 | tf_op jit(solution)/shard_map/ppermute | solution.py:33
  25.7 0.8 collective-permute-start.12
  27.6 6.4 %collective-permute-start.11 = (f32[64,256]{1,0:T(8,128)S(1)}, f32[64,256]{1,0:T(8,128)S(1)}, u32[]{:S(2)}, u32[]{:S(2)}) collective-permute-start(f32[64,256]{1,0:T(8,128)S(1)} %get-tuple-element.56), channel_id=1, source_target_pairs={{0,2},{1,3},{2,0},{3,1},{4,6},{5,7},{6,4},{7,5},{8,10},{9,11},{10,... | collective-permute-start | bytes 196616 | tf_op jit(solution)/shard_map/ppermute | solution.py:33
  35.4 3.3 %collective-permute-start.16 = (f32[64,256]{1,0:T(8,128)S(1)}, f32[64,256]{1,0:T(8,128)S(1)}, u32[]{:S(2)}, u32[]{:S(2)}) collective-permute-start(f32[64,256]{1,0:T(8,128)S(1)} %get-tuple-element.59), channel_id=1, source_target_pairs={{0,3},{1,2},{2,1},{3,0},{4,7},{5,6},{6,5},{7,4},{8,11},{9,10},{10,... | collective-permute-start | bytes 196616 | tf_op jit(solution)/shard_map/ppermute | solution.py:33
  39.3 1.1 collective-permute-done.11
  41.1 4.6 %collective-permute-start.19 = (f32[64,256]{1,0:T(8,128)S(1)}, f32[64,256]{1,0:T(8,128)S(1)}, u32[]{:S(2)}, u32[]{:S(2)}) collective-permute-start(f32[64,256]{1,0:T(8,128)S(1)} %get-tuple-element.61.refs_2_), channel_id=1, source_target_pairs={{0,2},{1,3},{2,0},{3,1},{4,6},{5,7},{6,4},{7,5},{8,10},{9,11},{10,... | collective-permute-start | bytes 196616 | tf_op jit(solution)/shard_map/ppermute | solution.py:33
  45.7 1.1 collective-permute-start.20
  46.9 1.2 collective-permute-done.17
  48.8 2.0 %collective-permute-start.21 = (f32[64,256]{1,0:T(8,128)S(1)}, f32[64,256]{1,0:T(8,128)S(1)}, u32[]{:S(2)}, u32[]{:S(2)}) collective-permute-start(f32[64,256]{1,0:T(8,128)S(1)} %get-tuple-element.65.refs_3_), channel_id=1, source_target_pairs={{0,3},{1,2},{2,1},{3,0},{4,7},{5,6},{6,5},{7,4},{8,11},{9,10},{10,... | collective-permute-start | bytes 196616 | tf_op jit(solution)/shard_map/ppermute | solution.py:33
  51.1 2.1 %collective-permute-start.24 = (f32[64,256]{1,0:T(8,128)S(1)}, f32[64,256]{1,0:T(8,128)S(1)}, u32[]{:S(2)}, u32[]{:S(2)}) collective-permute-start(f32[64,256]{1,0:T(8,128)S(1)} %get-tuple-element.65.refs_3_), channel_id=1, source_target_pairs={{0,1},{1,0},{2,3},{3,2},{4,5},{5,4},{6,7},{7,6},{8,9},{9,8},{10,11... | collective-permute-start | bytes 196616 | tf_op jit(solution)/shard_map/ppermute | solution.py:33
  53.2 1.9 %collective-permute-done.18 = f32[64,256]{1,0:T(8,128)S(1)} collective-permute-done((f32[64,256]{1,0:T(8,128)S(1)}, f32[64,256]{1,0:T(8,128)S(1)}, u32[]{:S(2)}, u32[]{:S(2)}) %collective-permute-start.18) | collective-permute-done | bytes 65568 | tf_op jit(solution)/shard_map/ppermute | solution.py:33
  55.9 2.1 %collective-permute-start.26 = (f32[64,256]{1,0:T(8,128)S(1)}, f32[64,256]{1,0:T(8,128)S(1)}, u32[]{:S(2)}, u32[]{:S(2)}) collective-permute-start(f32[64,256]{1,0:T(8,128)S(1)} %get-tuple-element.64), channel_id=1, source_target_pairs={{0,3},{1,2},{2,1},{3,0},{4,7},{5,6},{6,5},{7,4},{8,11},{9,10},{10,... | collective-permute-start | bytes 196616 | tf_op jit(solution)/shard_map/ppermute | solution.py:33
  58.0 1.4 %collective-permute-start.22 = (f32[64,256]{1,0:T(8,128)S(1)}, f32[64,256]{1,0:T(8,128)S(1)}, u32[]{:S(2)}, u32[]{:S(2)}) collective-permute-start(f32[64,256]{1,0:T(8,128)S(1)} %get-tuple-element.64), channel_id=1, source_target_pairs={{0,1},{1,0},{2,3},{3,2},{4,5},{5,4},{6,7},{7,6},{8,9},{9,8},{10,11... | collective-permute-start | bytes 196616 | tf_op jit(solution)/shard_map/ppermute | solution.py:33
  60.1 2.1 %collective-permute-start.28 = (f32[64,256]{1,0:T(8,128)S(1)}, f32[64,256]{1,0:T(8,128)S(1)}, u32[]{:S(2)}, u32[]{:S(2)}) collective-permute-start(f32[64,256]{1,0:T(8,128)S(1)} %get-tuple-element.67), channel_id=1, source_target_pairs={{0,3},{1,2},{2,1},{3,0},{4,7},{5,6},{6,5},{7,4},{8,11},{9,10},{10,... | collective-permute-start | bytes 196616 | tf_op jit(solution)/shard_map/ppermute | solution.py:33
  62.3 2.0 %collective-permute-done.23 = f32[64,256]{1,0:T(8,128)S(1)} collective-permute-done((f32[64,256]{1,0:T(8,128)S(1)}, f32[64,256]{1,0:T(8,128)S(1)}, u32[]{:S(2)}, u32[]{:S(2)}) %collective-permute-start.23) | collective-permute-done | bytes 65568 | tf_op jit(solution)/shard_map/ppermute | solution.py:33
  65.3 1.9 %collective-permute-start.31 = (f32[64,256]{1,0:T(8,128)S(1)}, f32[64,256]{1,0:T(8,128)S(1)}, u32[]{:S(2)}, u32[]{:S(2)}) collective-permute-start(f32[64,256]{1,0:T(8,128)S(1)} %get-tuple-element.69.refs_4_), channel_id=1, source_target_pairs={{0,2},{1,3},{2,0},{3,1},{4,6},{5,7},{6,4},{7,5},{8,10},{9,11},{10,... | collective-permute-start | bytes 196616 | tf_op jit(solution)/shard_map/ppermute | solution.py:33
  67.2 2.2 %collective-permute-start.32 = (f32[64,256]{1,0:T(8,128)S(1)}, f32[64,256]{1,0:T(8,128)S(1)}, u32[]{:S(2)}, u32[]{:S(2)}) collective-permute-start(f32[64,256]{1,0:T(8,128)S(1)} %get-tuple-element.69.refs_4_), channel_id=1, source_target_pairs={{0,3},{1,2},{2,1},{3,0},{4,7},{5,6},{6,5},{7,4},{8,11},{9,10},{10,... | collective-permute-start | bytes 196616 | tf_op jit(solution)/shard_map/ppermute | solution.py:33
  69.4 1.0 collective-permute-start.30
  70.4 1.5 %collective-permute-done.29 = f32[64,256]{1,0:T(8,128)S(1)} collective-permute-done((f32[64,256]{1,0:T(8,128)S(1)}, f32[64,256]{1,0:T(8,128)S(1)}, u32[]{:S(2)}, u32[]{:S(2)}) %collective-permute-start.29) | collective-permute-done | bytes 65568 | tf_op jit(solution)/shard_map/ppermute | solution.py:33
  72.6 1.8 %collective-permute-start.33 = (f32[64,256]{1,0:T(8,128)S(1)}, f32[64,256]{1,0:T(8,128)S(1)}, u32[]{:S(2)}, u32[]{:S(2)}) collective-permute-start(f32[64,256]{1,0:T(8,128)S(1)} %get-tuple-element.73.refs_5_), channel_id=1, source_target_pairs={{0,3},{1,2},{2,1},{3,0},{4,7},{5,6},{6,5},{7,4},{8,11},{9,10},{10,... | collective-permute-start | bytes 196616 | tf_op jit(solution)/shard_map/ppermute | solution.py:33
  74.4 1.1 collective-permute-done.31
  75.5 1.6 %collective-permute-start.36 = (f32[64,256]{1,0:T(8,128)S(1)}, f32[64,256]{1,0:T(8,128)S(1)}, u32[]{:S(2)}, u32[]{:S(2)}) collective-permute-start(f32[64,256]{1,0:T(8,128)S(1)} %get-tuple-element.73.refs_5_), channel_id=1, source_target_pairs={{0,1},{1,0},{2,3},{3,2},{4,5},{5,4},{6,7},{7,6},{8,9},{9,8},{10,11... | collective-permute-start | bytes 196616 | tf_op jit(solution)/shard_map/ppermute | solution.py:33
  78.5 2.2 %collective-permute-start.38 = (f32[64,256]{1,0:T(8,128)S(1)}, f32[64,256]{1,0:T(8,128)S(1)}, u32[]{:S(2)}, u32[]{:S(2)}) collective-permute-start(f32[64,256]{1,0:T(8,128)S(1)} %get-tuple-element.72), channel_id=1, source_target_pairs={{0,3},{1,2},{2,1},{3,0},{4,7},{5,6},{6,5},{7,4},{8,11},{9,10},{10,... | collective-permute-start | bytes 196616 | tf_op jit(solution)/shard_map/ppermute | solution.py:33
  80.7 0.9 collective-permute-start.34
  81.7 2.3 %collective-permute-done.37 = f32[64,256]{1,0:T(8,128)S(1)} collective-permute-done((f32[64,256]{1,0:T(8,128)S(1)}, f32[64,256]{1,0:T(8,128)S(1)}, u32[]{:S(2)}, u32[]{:S(2)}) %collective-permute-start.37) | collective-permute-done | bytes 65568 | tf_op jit(solution)/shard_map/ppermute | solution.py:33
  84.6 3.0 %collective-permute-start.40 = (f32[64,256]{1,0:T(8,128)S(1)}, f32[64,256]{1,0:T(8,128)S(1)}, u32[]{:S(2)}, u32[]{:S(2)}) collective-permute-start(f32[64,256]{1,0:T(8,128)S(1)} %get-tuple-element.75), channel_id=1, source_target_pairs={{0,3},{1,2},{2,1},{3,0},{4,7},{5,6},{6,5},{7,4},{8,11},{9,10},{10,... | collective-permute-start | bytes 196616 | tf_op jit(solution)/shard_map/ppermute | solution.py:33
  87.7 1.4 %collective-permute-start.39 = (f32[64,256]{1,0:T(8,128)S(1)}, f32[64,256]{1,0:T(8,128)S(1)}, u32[]{:S(2)}, u32[]{:S(2)}) collective-permute-start(f32[64,256]{1,0:T(8,128)S(1)} %get-tuple-element.75), channel_id=1, source_target_pairs={{0,1},{1,0},{2,3},{3,2},{4,5},{5,4},{6,7},{7,6},{8,9},{9,8},{10,11... | collective-permute-start | bytes 196616 | tf_op jit(solution)/shard_map/ppermute | solution.py:33
  89.8 1.6 %collective-permute-start.43 = (f32[64,256]{1,0:T(8,128)S(1)}, f32[64,256]{1,0:T(8,128)S(1)}, u32[]{:S(2)}, u32[]{:S(2)}) collective-permute-start(f32[64,256]{1,0:T(8,128)S(1)} %get-tuple-element.77.refs_6_), channel_id=1, source_target_pairs={{0,2},{1,3},{2,0},{3,1},{4,6},{5,7},{6,4},{7,5},{8,10},{9,11},{10,... | collective-permute-start | bytes 196616 | tf_op jit(solution)/shard_map/ppermute | solution.py:33
  91.4 1.5 %collective-permute-start.44 = (f32[64,256]{1,0:T(8,128)S(1)}, f32[64,256]{1,0:T(8,128)S(1)}, u32[]{:S(2)}, u32[]{:S(2)}) collective-permute-start(f32[64,256]{1,0:T(8,128)S(1)} %get-tuple-element.77.refs_6_), channel_id=1, source_target_pairs={{0,3},{1,2},{2,1},{3,0},{4,7},{5,6},{6,5},{7,4},{8,11},{9,10},{10,... | collective-permute-start | bytes 196616 | tf_op jit(solution)/shard_map/ppermute | solution.py:33
  93.4 1.0 collective-permute-done.39
  95.1 1.4 %collective-permute-start.46 = (f32[64,256]{1,0:T(8,128)S(1)}, f32[64,256]{1,0:T(8,128)S(1)}, u32[]{:S(2)}, u32[]{:S(2)}) collective-permute-start(f32[64,256]{1,0:T(8,128)S(1)} %get-tuple-element.79.refs_7_), channel_id=1, source_target_pairs={{0,2},{1,3},{2,0},{3,1},{4,6},{5,7},{6,4},{7,5},{8,10},{9,11},{10,... | collective-permute-start | bytes 196616 | tf_op jit(solution)/shard_map/ppermute | solution.py:33
  96.6 1.5 %collective-permute-start.47 = (f32[64,256]{1,0:T(8,128)S(1)}, f32[64,256]{1,0:T(8,128)S(1)}, u32[]{:S(2)}, u32[]{:S(2)}) collective-permute-start(f32[64,256]{1,0:T(8,128)S(1)} %get-tuple-element.79.refs_7_), channel_id=1, source_target_pairs={{0,3},{1,2},{2,1},{3,0},{4,7},{5,6},{6,5},{7,4},{8,11},{9,10},{10,... | collective-permute-start | bytes 196616 | tf_op jit(solution)/shard_map/ppermute | solution.py:33
  98.8 2.3 %collective-permute-done.46 = f32[64,256]{1,0:T(8,128)S(1)} collective-permute-done((f32[64,256]{1,0:T(8,128)S(1)}, f32[64,256]{1,0:T(8,128)S(1)}, u32[]{:S(2)}, u32[]{:S(2)}) %collective-permute-start.46) | collective-permute-done | bytes 65568 | tf_op jit(solution)/shard_map/ppermute | solution.py:33
  101.1 1.2 shard_map.117.refs_0_
  102.3 0.8 collective-permute-done.45
  103.1 1.2 shard_map.118
  104.4 1.3 collective-permute-done.48.refs_1_
  105.8 2.5 %collective-permute-start.49 = (f32[2,16,512]{2,1,0:T(8,128)S(1)}, f32[2,16,512]{2,1,0:T(8,128)S(1)}, u32[]{:S(2)}, u32[]{:S(2)}) collective-permute-start(f32[2,16,512]{2,1,0:T(8,128)S(1)} %get-tuple-element.85), channel_id=1, source_target_pairs={{0,24},{4,28},{8,16},{12,20},{16,8},{20,12},{24,0},{28,4},{1,25},{... | collective-permute-start | bytes 196616 | tf_op jit(solution)/shard_map/ppermute | solution.py:83
  109.3 1.0 shard_map.119
  111.0 1.5 %collective-permute-done.50.refs_2_ = f32[2,16,512]{2,1,0:T(8,128)S(1)} collective-permute-done((f32[2,16,512]{2,1,0:T(8,128)S(1)}, f32[2,16,512]{2,1,0:T(8,128)S(1)}, u32[]{:S(2)}, u32[]{:S(2)}) %collective-permute-start.50) | collective-permute-done | bytes 65568 | tf_op jit(solution)/shard_map/ppermute | solution.py:83
  113.5 0.9 collective-permute-start.52
  114.4 1.5 %collective-permute-start.53 = (f32[16,1024]{1,0:T(8,128)S(1)}, f32[16,1024]{1,0:T(8,128)S(1)}, u32[]{:S(2)}, u32[]{:S(2)}) collective-permute-start(f32[16,1024]{1,0:T(8,128)S(1)} %get-tuple-element.89.refs_2_.refs_0_), channel_id=1, source_target_pairs={{0,3},{1,2},{2,1},{3,0},{4,7},{5,6},{6,5},{7,4},{8,11},{9,10},{10,... | collective-permute-start | bytes 196616 | tf_op jit(solution)/shard_map/ppermute | solution.py:33
  115.9 1.1 collective-permute-start.54
  117.5 1.7 %collective-permute-done.52.refs_1_ = f32[16,1024]{1,0:T(8,128)S(1)} collective-permute-done((f32[16,1024]{1,0:T(8,128)S(1)}, f32[16,1024]{1,0:T(8,128)S(1)}, u32[]{:S(2)}, u32[]{:S(2)}) %collective-permute-start.52) | collective-permute-done | bytes 65568 | tf_op jit(solution)/shard_map/ppermute | solution.py:33
  119.2 1.4 %collective-permute-done.53.refs_2_ = f32[16,1024]{1,0:T(8,128)S(1)} collective-permute-done((f32[16,1024]{1,0:T(8,128)S(1)}, f32[16,1024]{1,0:T(8,128)S(1)}, u32[]{:S(2)}, u32[]{:S(2)}) %collective-permute-start.53) | collective-permute-done | bytes 65568 | tf_op jit(solution)/shard_map/ppermute | solution.py:33
  121.2 1.2 collective-permute-start.55
  122.4 1.6 %collective-permute-start.56 = (f32[16,512]{1,0:T(8,128)S(1)}, f32[16,512]{1,0:T(8,128)S(1)}, u32[]{:S(2)}, u32[]{:S(2)}) collective-permute-start(f32[16,512]{1,0:T(8,128)S(1)} %get-tuple-element.98), channel_id=1, source_target_pairs={{0,3},{1,2},{2,1},{3,0},{4,7},{5,6},{6,5},{7,4},{8,11},{9,10},{10,... | collective-permute-start | bytes 98312 | tf_op jit(solution)/shard_map/ppermute | solution.py:33
  124.8 1.5 %collective-permute-done.55.refs_2_ = f32[16,512]{1,0:T(8,128)S(1)} collective-permute-done((f32[16,512]{1,0:T(8,128)S(1)}, f32[16,512]{1,0:T(8,128)S(1)}, u32[]{:S(2)}, u32[]{:S(2)}) %collective-permute-start.55) | collective-permute-done | bytes 32800 | tf_op jit(solution)/shard_map/ppermute | solution.py:33
  126.3 2.0 %collective-permute-done.56.refs_3_ = f32[16,512]{1,0:T(8,128)S(1)} collective-permute-done((f32[16,512]{1,0:T(8,128)S(1)}, f32[16,512]{1,0:T(8,128)S(1)}, u32[]{:S(2)}, u32[]{:S(2)}) %collective-permute-start.56) | collective-permute-done | bytes 32800 | tf_op jit(solution)/shard_map/ppermute | solution.py:33
  128.7 1.0 collective-permute-start.58
  129.7 1.8 %collective-permute-start.59 = (f32[16,256]{1,0:T(8,128)S(1)}, f32[16,256]{1,0:T(8,128)S(1)}, u32[]{:S(2)}, u32[]{:S(2)}) collective-permute-start(f32[16,256]{1,0:T(8,128)S(1)} %shard_map.124.refs_0_), channel_id=1, source_target_pairs={{0,3},{1,2},{2,1},{3,0},{4,7},{5,6},{6,5},{7,4},{8,11},{9,10},{10,... | collective-permute-start | bytes 49160 | tf_op jit(solution)/shard_map/ppermute | solution.py:33
  132.2 1.2 collective-permute-done.58.refs_1_
  133.4 1.8 %collective-permute-done.59.refs_2_ = f32[16,256]{1,0:T(8,128)S(1)} collective-permute-done((f32[16,256]{1,0:T(8,128)S(1)}, f32[16,256]{1,0:T(8,128)S(1)}, u32[]{:S(2)}, u32[]{:S(2)}) %collective-permute-start.59) | collective-permute-done | bytes 16416 | tf_op jit(solution)/shard_map/ppermute | solution.py:33
  135.4 1.0 shard_map.125
  (162 shorter events, 19.7 us)
Async XLA Ops:
  1.7 24.8 %copy-start.3 = (f32[1,4,256,128]{3,2,1,0:T(8,128)S(1)}, f32[1,4,256,128]{3,2,1,0:T(8,128)}, u32[]{:S(2)}) copy-start(f32[1,4,256,128]{3,2,1,0:T(8,128)} %rhs_ref.3) | copy-start | bytes 1572868
  1.9 10.1 %collective-permute-start = (f32[64,256]{1,0:T(8,128)S(1)}, f32[64,256]{1,0:T(8,128)S(1)}, u32[]{:S(2)}, u32[]{:S(2)}) collective-permute-start(f32[64,256]{1,0:T(8,128)S(1)} %get-tuple-element.52.refs_0_), channel_id=1, source_target_pairs={{0,1},{1,0},{2,3},{3,2},{4,5},{5,4},{6,7},{7,6},{8,9},{9,8},{10,11... | collective-permute-start | bytes 196616 | tf_op jit(solution)/shard_map/ppermute | solution.py:33
  5.0 9.1 %collective-permute-start.1 = (f32[64,256]{1,0:T(8,128)S(1)}, f32[64,256]{1,0:T(8,128)S(1)}, u32[]{:S(2)}, u32[]{:S(2)}) collective-permute-start(f32[64,256]{1,0:T(8,128)S(1)} %get-tuple-element.52.refs_0_), channel_id=1, source_target_pairs={{0,2},{1,3},{2,0},{3,1},{4,6},{5,7},{6,4},{7,5},{8,10},{9,11},{10,... | collective-permute-start | bytes 196616 | tf_op jit(solution)/shard_map/ppermute | solution.py:33
  7.6 6.6 %collective-permute-start.2 = (f32[64,256]{1,0:T(8,128)S(1)}, f32[64,256]{1,0:T(8,128)S(1)}, u32[]{:S(2)}, u32[]{:S(2)}) collective-permute-start(f32[64,256]{1,0:T(8,128)S(1)} %get-tuple-element.52.refs_0_), channel_id=1, source_target_pairs={{0,3},{1,2},{2,1},{3,0},{4,7},{5,6},{6,5},{7,4},{8,11},{9,10},{10,... | collective-permute-start | bytes 196616 | tf_op jit(solution)/shard_map/ppermute | solution.py:33
  7.6 12.2 %collective-permute-start.3 = (f32[64,256]{1,0:T(8,128)S(1)}, f32[64,256]{1,0:T(8,128)S(1)}, u32[]{:S(2)}, u32[]{:S(2)}) collective-permute-start(f32[64,256]{1,0:T(8,128)S(1)} %get-tuple-element.53.refs_0_), channel_id=1, source_target_pairs={{0,1},{1,0},{2,3},{3,2},{4,5},{5,4},{6,7},{7,6},{8,9},{9,8},{10,11... | collective-permute-start | bytes 196616 | tf_op jit(solution)/shard_map/ppermute | solution.py:33
  8.5 12.7 %collective-permute-start.4 = (f32[64,256]{1,0:T(8,128)S(1)}, f32[64,256]{1,0:T(8,128)S(1)}, u32[]{:S(2)}, u32[]{:S(2)}) collective-permute-start(f32[64,256]{1,0:T(8,128)S(1)} %get-tuple-element.53.refs_0_), channel_id=1, source_target_pairs={{0,2},{1,3},{2,0},{3,1},{4,6},{5,7},{6,4},{7,5},{8,10},{9,11},{10,... | collective-permute-start | bytes 196616 | tf_op jit(solution)/shard_map/ppermute | solution.py:33
  12.0 9.2 %collective-permute-start.5 = (f32[64,256]{1,0:T(8,128)S(1)}, f32[64,256]{1,0:T(8,128)S(1)}, u32[]{:S(2)}, u32[]{:S(2)}) collective-permute-start(f32[64,256]{1,0:T(8,128)S(1)} %get-tuple-element.53.refs_0_), channel_id=1, source_target_pairs={{0,3},{1,2},{2,1},{3,0},{4,7},{5,6},{6,5},{7,4},{8,11},{9,10},{10,... | collective-permute-start | bytes 196616 | tf_op jit(solution)/shard_map/ppermute | solution.py:33
  14.6 11.9 %collective-permute-start.6 = (f32[64,256]{1,0:T(8,128)S(1)}, f32[64,256]{1,0:T(8,128)S(1)}, u32[]{:S(2)}, u32[]{:S(2)}) collective-permute-start(f32[64,256]{1,0:T(8,128)S(1)} %shard_map.114.refs_0_), channel_id=1, source_target_pairs={{0,1},{1,0},{2,3},{3,2},{4,5},{5,4},{6,7},{7,6},{8,9},{9,8},{10,11... | collective-permute-start | bytes 196616 | tf_op jit(solution)/shard_map/ppermute | solution.py:33
  17.7 8.0 %collective-permute-start.7 = (f32[64,256]{1,0:T(8,128)S(1)}, f32[64,256]{1,0:T(8,128)S(1)}, u32[]{:S(2)}, u32[]{:S(2)}) collective-permute-start(f32[64,256]{1,0:T(8,128)S(1)} %shard_map.114.refs_0_), channel_id=1, source_target_pairs={{0,2},{1,3},{2,0},{3,1},{4,6},{5,7},{6,4},{7,5},{8,10},{9,11},{10,... | collective-permute-start | bytes 196616 | tf_op jit(solution)/shard_map/ppermute | solution.py:33
  19.8 7.1 %collective-permute-start.8 = (f32[64,256]{1,0:T(8,128)S(1)}, f32[64,256]{1,0:T(8,128)S(1)}, u32[]{:S(2)}, u32[]{:S(2)}) collective-permute-start(f32[64,256]{1,0:T(8,128)S(1)} %shard_map.114.refs_0_), channel_id=1, source_target_pairs={{0,3},{1,2},{2,1},{3,0},{4,7},{5,6},{6,5},{7,4},{8,11},{9,10},{10,... | collective-permute-start | bytes 196616 | tf_op jit(solution)/shard_map/ppermute | solution.py:33
  21.7 12.3 %collective-permute-start.9 = (f32[64,256]{1,0:T(8,128)S(1)}, f32[64,256]{1,0:T(8,128)S(1)}, u32[]{:S(2)}, u32[]{:S(2)}) collective-permute-start(f32[64,256]{1,0:T(8,128)S(1)} %shard_map.115.refs_1_), channel_id=1, source_target_pairs={{0,3},{1,2},{2,1},{3,0},{4,7},{5,6},{6,5},{7,4},{8,11},{9,10},{10,... | collective-permute-start | bytes 196616 | tf_op jit(solution)/shard_map/ppermute | solution.py:33
  24.2 10.5 %collective-permute-start.13 = (f32[64,256]{1,0:T(8,128)S(1)}, f32[64,256]{1,0:T(8,128)S(1)}, u32[]{:S(2)}, u32[]{:S(2)}) collective-permute-start(f32[64,256]{1,0:T(8,128)S(1)} %shard_map.115.refs_1_), channel_id=1, source_target_pairs={{0,2},{1,3},{2,0},{3,1},{4,6},{5,7},{6,4},{7,5},{8,10},{9,11},{10,... | collective-permute-start | bytes 196616 | tf_op jit(solution)/shard_map/ppermute | solution.py:33
  25.7 9.0 %collective-permute-start.12 = (f32[64,256]{1,0:T(8,128)S(1)}, f32[64,256]{1,0:T(8,128)S(1)}, u32[]{:S(2)}, u32[]{:S(2)}) collective-permute-start(f32[64,256]{1,0:T(8,128)S(1)} %shard_map.115.refs_1_), channel_id=1, source_target_pairs={{0,1},{1,0},{2,3},{3,2},{4,5},{5,4},{6,7},{7,6},{8,9},{9,8},{10,11... | collective-permute-start | bytes 196616 | tf_op jit(solution)/shard_map/ppermute | solution.py:33
  27.6 12.8 %collective-permute-start.11 = (f32[64,256]{1,0:T(8,128)S(1)}, f32[64,256]{1,0:T(8,128)S(1)}, u32[]{:S(2)}, u32[]{:S(2)}) collective-permute-start(f32[64,256]{1,0:T(8,128)S(1)} %get-tuple-element.56), channel_id=1, source_target_pairs={{0,2},{1,3},{2,0},{3,1},{4,6},{5,7},{6,4},{7,5},{8,10},{9,11},{10,... | collective-permute-start | bytes 196616 | tf_op jit(solution)/shard_map/ppermute | solution.py:33
  34.0 6.4 %collective-permute-start.14 = (f32[64,256]{1,0:T(8,128)S(1)}, f32[64,256]{1,0:T(8,128)S(1)}, u32[]{:S(2)}, u32[]{:S(2)}) collective-permute-start(f32[64,256]{1,0:T(8,128)S(1)} %get-tuple-element.56), channel_id=1, source_target_pairs={{0,3},{1,2},{2,1},{3,0},{4,7},{5,6},{6,5},{7,4},{8,11},{9,10},{10,... | collective-permute-start | bytes 196616 | tf_op jit(solution)/shard_map/ppermute | solution.py:33
  34.0 6.4 %collective-permute-start.10 = (f32[64,256]{1,0:T(8,128)S(1)}, f32[64,256]{1,0:T(8,128)S(1)}, u32[]{:S(2)}, u32[]{:S(2)}) collective-permute-start(f32[64,256]{1,0:T(8,128)S(1)} %get-tuple-element.56), channel_id=1, source_target_pairs={{0,1},{1,0},{2,3},{3,2},{4,5},{5,4},{6,7},{7,6},{8,9},{9,8},{10,11... | collective-permute-start | bytes 196616 | tf_op jit(solution)/shard_map/ppermute | solution.py:33
  35.4 11.5 %collective-permute-start.16 = (f32[64,256]{1,0:T(8,128)S(1)}, f32[64,256]{1,0:T(8,128)S(1)}, u32[]{:S(2)}, u32[]{:S(2)}) collective-permute-start(f32[64,256]{1,0:T(8,128)S(1)} %get-tuple-element.59), channel_id=1, source_target_pairs={{0,3},{1,2},{2,1},{3,0},{4,7},{5,6},{6,5},{7,4},{8,11},{9,10},{10,... | collective-permute-start | bytes 196616 | tf_op jit(solution)/shard_map/ppermute | solution.py:33
  38.6 9.5 %collective-permute-start.17 = (f32[64,256]{1,0:T(8,128)S(1)}, f32[64,256]{1,0:T(8,128)S(1)}, u32[]{:S(2)}, u32[]{:S(2)}) collective-permute-start(f32[64,256]{1,0:T(8,128)S(1)} %get-tuple-element.59), channel_id=1, source_target_pairs={{0,2},{1,3},{2,0},{3,1},{4,6},{5,7},{6,4},{7,5},{8,10},{9,11},{10,... | collective-permute-start | bytes 196616 | tf_op jit(solution)/shard_map/ppermute | solution.py:33
  40.4 6.5 %collective-permute-start.15 = (f32[64,256]{1,0:T(8,128)S(1)}, f32[64,256]{1,0:T(8,128)S(1)}, u32[]{:S(2)}, u32[]{:S(2)}) collective-permute-start(f32[64,256]{1,0:T(8,128)S(1)} %get-tuple-element.59), channel_id=1, source_target_pairs={{0,1},{1,0},{2,3},{3,2},{4,5},{5,4},{6,7},{7,6},{8,9},{9,8},{10,11... | collective-permute-start | bytes 196616 | tf_op jit(solution)/shard_map/ppermute | solution.py:33
  41.1 10.0 %collective-permute-start.19 = (f32[64,256]{1,0:T(8,128)S(1)}, f32[64,256]{1,0:T(8,128)S(1)}, u32[]{:S(2)}, u32[]{:S(2)}) collective-permute-start(f32[64,256]{1,0:T(8,128)S(1)} %get-tuple-element.61.refs_2_), channel_id=1, source_target_pairs={{0,2},{1,3},{2,0},{3,1},{4,6},{5,7},{6,4},{7,5},{8,10},{9,11},{10,... | collective-permute-start | bytes 196616 | tf_op jit(solution)/shard_map/ppermute | solution.py:33
  45.7 9.4 %collective-permute-start.20 = (f32[64,256]{1,0:T(8,128)S(1)}, f32[64,256]{1,0:T(8,128)S(1)}, u32[]{:S(2)}, u32[]{:S(2)}) collective-permute-start(f32[64,256]{1,0:T(8,128)S(1)} %get-tuple-element.61.refs_2_), channel_id=1, source_target_pairs={{0,3},{1,2},{2,1},{3,0},{4,7},{5,6},{6,5},{7,4},{8,11},{9,10},{10,... | collective-permute-start | bytes 196616 | tf_op jit(solution)/shard_map/ppermute | solution.py:33
  46.9 8.3 %collective-permute-start.18 = (f32[64,256]{1,0:T(8,128)S(1)}, f32[64,256]{1,0:T(8,128)S(1)}, u32[]{:S(2)}, u32[]{:S(2)}) collective-permute-start(f32[64,256]{1,0:T(8,128)S(1)} %get-tuple-element.61.refs_2_), channel_id=1, source_target_pairs={{0,1},{1,0},{2,3},{3,2},{4,5},{5,4},{6,7},{7,6},{8,9},{9,8},{10,11... | collective-permute-start | bytes 196616 | tf_op jit(solution)/shard_map/ppermute | solution.py:33
  48.8 9.2 %collective-permute-start.21 = (f32[64,256]{1,0:T(8,128)S(1)}, f32[64,256]{1,0:T(8,128)S(1)}, u32[]{:S(2)}, u32[]{:S(2)}) collective-permute-start(f32[64,256]{1,0:T(8,128)S(1)} %get-tuple-element.65.refs_3_), channel_id=1, source_target_pairs={{0,3},{1,2},{2,1},{3,0},{4,7},{5,6},{6,5},{7,4},{8,11},{9,10},{10,... | collective-permute-start | bytes 196616 | tf_op jit(solution)/shard_map/ppermute | solution.py:33
  50.8 8.6 %collective-permute-start.25 = (f32[64,256]{1,0:T(8,128)S(1)}, f32[64,256]{1,0:T(8,128)S(1)}, u32[]{:S(2)}, u32[]{:S(2)}) collective-permute-start(f32[64,256]{1,0:T(8,128)S(1)} %get-tuple-element.65.refs_3_), channel_id=1, source_target_pairs={{0,2},{1,3},{2,0},{3,1},{4,6},{5,7},{6,4},{7,5},{8,10},{9,11},{10,... | collective-permute-start | bytes 196616 | tf_op jit(solution)/shard_map/ppermute | solution.py:33
  51.1 8.3 %collective-permute-start.24 = (f32[64,256]{1,0:T(8,128)S(1)}, f32[64,256]{1,0:T(8,128)S(1)}, u32[]{:S(2)}, u32[]{:S(2)}) collective-permute-start(f32[64,256]{1,0:T(8,128)S(1)} %get-tuple-element.65.refs_3_), channel_id=1, source_target_pairs={{0,1},{1,0},{2,3},{3,2},{4,5},{5,4},{6,7},{7,6},{8,9},{9,8},{10,11... | collective-permute-start | bytes 196616 | tf_op jit(solution)/shard_map/ppermute | solution.py:33
  55.9 8.4 %collective-permute-start.23 = (f32[64,256]{1,0:T(8,128)S(1)}, f32[64,256]{1,0:T(8,128)S(1)}, u32[]{:S(2)}, u32[]{:S(2)}) collective-permute-start(f32[64,256]{1,0:T(8,128)S(1)} %get-tuple-element.64), channel_id=1, source_target_pairs={{0,2},{1,3},{2,0},{3,1},{4,6},{5,7},{6,4},{7,5},{8,10},{9,11},{10,... | collective-permute-start | bytes 196616 | tf_op jit(solution)/shard_map/ppermute | solution.py:33
  55.9 8.7 %collective-permute-start.26 = (f32[64,256]{1,0:T(8,128)S(1)}, f32[64,256]{1,0:T(8,128)S(1)}, u32[]{:S(2)}, u32[]{:S(2)}) collective-permute-start(f32[64,256]{1,0:T(8,128)S(1)} %get-tuple-element.64), channel_id=1, source_target_pairs={{0,3},{1,2},{2,1},{3,0},{4,7},{5,6},{6,5},{7,4},{8,11},{9,10},{10,... | collective-permute-start | bytes 196616 | tf_op jit(solution)/shard_map/ppermute | solution.py:33
  58.0 6.6 %collective-permute-start.22 = (f32[64,256]{1,0:T(8,128)S(1)}, f32[64,256]{1,0:T(8,128)S(1)}, u32[]{:S(2)}, u32[]{:S(2)}) collective-permute-start(f32[64,256]{1,0:T(8,128)S(1)} %get-tuple-element.64), channel_id=1, source_target_pairs={{0,1},{1,0},{2,3},{3,2},{4,5},{5,4},{6,7},{7,6},{8,9},{9,8},{10,11... | collective-permute-start | bytes 196616 | tf_op jit(solution)/shard_map/ppermute | solution.py:33
  60.1 9.3 %collective-permute-start.28 = (f32[64,256]{1,0:T(8,128)S(1)}, f32[64,256]{1,0:T(8,128)S(1)}, u32[]{:S(2)}, u32[]{:S(2)}) collective-permute-start(f32[64,256]{1,0:T(8,128)S(1)} %get-tuple-element.67), channel_id=1, source_target_pairs={{0,3},{1,2},{2,1},{3,0},{4,7},{5,6},{6,5},{7,4},{8,11},{9,10},{10,... | collective-permute-start | bytes 196616 | tf_op jit(solution)/shard_map/ppermute | solution.py:33
  62.2 9.7 %collective-permute-start.29 = (f32[64,256]{1,0:T(8,128)S(1)}, f32[64,256]{1,0:T(8,128)S(1)}, u32[]{:S(2)}, u32[]{:S(2)}) collective-permute-start(f32[64,256]{1,0:T(8,128)S(1)} %get-tuple-element.67), channel_id=1, source_target_pairs={{0,2},{1,3},{2,0},{3,1},{4,6},{5,7},{6,4},{7,5},{8,10},{9,11},{10,... | collective-permute-start | bytes 196616 | tf_op jit(solution)/shard_map/ppermute | solution.py:33
  64.3 6.1 %collective-permute-start.27 = (f32[64,256]{1,0:T(8,128)S(1)}, f32[64,256]{1,0:T(8,128)S(1)}, u32[]{:S(2)}, u32[]{:S(2)}) collective-permute-start(f32[64,256]{1,0:T(8,128)S(1)} %get-tuple-element.67), channel_id=1, source_target_pairs={{0,1},{1,0},{2,3},{3,2},{4,5},{5,4},{6,7},{7,6},{8,9},{9,8},{10,11... | collective-permute-start | bytes 196616 | tf_op jit(solution)/shard_map/ppermute | solution.py:33
  65.3 10.2 %collective-permute-start.31 = (f32[64,256]{1,0:T(8,128)S(1)}, f32[64,256]{1,0:T(8,128)S(1)}, u32[]{:S(2)}, u32[]{:S(2)}) collective-permute-start(f32[64,256]{1,0:T(8,128)S(1)} %get-tuple-element.69.refs_4_), channel_id=1, source_target_pairs={{0,2},{1,3},{2,0},{3,1},{4,6},{5,7},{6,4},{7,5},{8,10},{9,11},{10,... | collective-permute-start | bytes 196616 | tf_op jit(solution)/shard_map/ppermute | solution.py:33
  67.2 9.9 %collective-permute-start.32 = (f32[64,256]{1,0:T(8,128)S(1)}, f32[64,256]{1,0:T(8,128)S(1)}, u32[]{:S(2)}, u32[]{:S(2)}) collective-permute-start(f32[64,256]{1,0:T(8,128)S(1)} %get-tuple-element.69.refs_4_), channel_id=1, source_target_pairs={{0,3},{1,2},{2,1},{3,0},{4,7},{5,6},{6,5},{7,4},{8,11},{9,10},{10,... | collective-permute-start | bytes 196616 | tf_op jit(solution)/shard_map/ppermute | solution.py:33
  69.4 7.6 %collective-permute-start.30 = (f32[64,256]{1,0:T(8,128)S(1)}, f32[64,256]{1,0:T(8,128)S(1)}, u32[]{:S(2)}, u32[]{:S(2)}) collective-permute-start(f32[64,256]{1,0:T(8,128)S(1)} %get-tuple-element.69.refs_4_), channel_id=1, source_target_pairs={{0,1},{1,0},{2,3},{3,2},{4,5},{5,4},{6,7},{7,6},{8,9},{9,8},{10,11... | collective-permute-start | bytes 196616 | tf_op jit(solution)/shard_map/ppermute | solution.py:33
  72.6 8.1 %collective-permute-start.33 = (f32[64,256]{1,0:T(8,128)S(1)}, f32[64,256]{1,0:T(8,128)S(1)}, u32[]{:S(2)}, u32[]{:S(2)}) collective-permute-start(f32[64,256]{1,0:T(8,128)S(1)} %get-tuple-element.73.refs_5_), channel_id=1, source_target_pairs={{0,3},{1,2},{2,1},{3,0},{4,7},{5,6},{6,5},{7,4},{8,11},{9,10},{10,... | collective-permute-start | bytes 196616 | tf_op jit(solution)/shard_map/ppermute | solution.py:33
  74.4 9.5 %collective-permute-start.37 = (f32[64,256]{1,0:T(8,128)S(1)}, f32[64,256]{1,0:T(8,128)S(1)}, u32[]{:S(2)}, u32[]{:S(2)}) collective-permute-start(f32[64,256]{1,0:T(8,128)S(1)} %get-tuple-element.73.refs_5_), channel_id=1, source_target_pairs={{0,2},{1,3},{2,0},{3,1},{4,6},{5,7},{6,4},{7,5},{8,10},{9,11},{10,... | collective-permute-start | bytes 196616 | tf_op jit(solution)/shard_map/ppermute | solution.py:33
  75.5 6.1 %collective-permute-start.36 = (f32[64,256]{1,0:T(8,128)S(1)}, f32[64,256]{1,0:T(8,128)S(1)}, u32[]{:S(2)}, u32[]{:S(2)}) collective-permute-start(f32[64,256]{1,0:T(8,128)S(1)} %get-tuple-element.73.refs_5_), channel_id=1, source_target_pairs={{0,1},{1,0},{2,3},{3,2},{4,5},{5,4},{6,7},{7,6},{8,9},{9,8},{10,11... | collective-permute-start | bytes 196616 | tf_op jit(solution)/shard_map/ppermute | solution.py:33
  77.8 9.9 %collective-permute-start.35 = (f32[64,256]{1,0:T(8,128)S(1)}, f32[64,256]{1,0:T(8,128)S(1)}, u32[]{:S(2)}, u32[]{:S(2)}) collective-permute-start(f32[64,256]{1,0:T(8,128)S(1)} %get-tuple-element.72), channel_id=1, source_target_pairs={{0,2},{1,3},{2,0},{3,1},{4,6},{5,7},{6,4},{7,5},{8,10},{9,11},{10,... | collective-permute-start | bytes 196616 | tf_op jit(solution)/shard_map/ppermute | solution.py:33
  78.5 10.6 %collective-permute-start.38 = (f32[64,256]{1,0:T(8,128)S(1)}, f32[64,256]{1,0:T(8,128)S(1)}, u32[]{:S(2)}, u32[]{:S(2)}) collective-permute-start(f32[64,256]{1,0:T(8,128)S(1)} %get-tuple-element.72), channel_id=1, source_target_pairs={{0,3},{1,2},{2,1},{3,0},{4,7},{5,6},{6,5},{7,4},{8,11},{9,10},{10,... | collective-permute-start | bytes 196616 | tf_op jit(solution)/shard_map/ppermute | solution.py:33
  80.7 8.4 %collective-permute-start.34 = (f32[64,256]{1,0:T(8,128)S(1)}, f32[64,256]{1,0:T(8,128)S(1)}, u32[]{:S(2)}, u32[]{:S(2)}) collective-permute-start(f32[64,256]{1,0:T(8,128)S(1)} %get-tuple-element.72), channel_id=1, source_target_pairs={{0,1},{1,0},{2,3},{3,2},{4,5},{5,4},{6,7},{7,6},{8,9},{9,8},{10,11... | collective-permute-start | bytes 196616 | tf_op jit(solution)/shard_map/ppermute | solution.py:33
  83.9 17.1 %copy-start = (f32[1,1,3,128,1024]{4,3,2,1,0:T(8,128)S(1)}, f32[1,1,3,128,1024]{4,3,2,1,0:T(8,128)}, u32[]{:S(2)}) copy-start(f32[1,1,3,128,1024]{4,3,2,1,0:T(8,128)} %param.13) | copy-start | bytes 4718596
  84.0 17.1 %copy-start.6 = (s32[1,1,3]{2,1,0:T(1,128)S(1)}, s32[1,1,3]{2,1,0:T(1,128)}, u32[]{:S(2)}) copy-start(s32[1,1,3]{2,1,0:T(1,128)} %refs_6_.1) | copy-start | bytes 40
  84.6 8.3 %collective-permute-start.40 = (f32[64,256]{1,0:T(8,128)S(1)}, f32[64,256]{1,0:T(8,128)S(1)}, u32[]{:S(2)}, u32[]{:S(2)}) collective-permute-start(f32[64,256]{1,0:T(8,128)S(1)} %get-tuple-element.75), channel_id=1, source_target_pairs={{0,3},{1,2},{2,1},{3,0},{4,7},{5,6},{6,5},{7,4},{8,11},{9,10},{10,... | collective-permute-start | bytes 196616 | tf_op jit(solution)/shard_map/ppermute | solution.py:33
  87.7 6.8 %collective-permute-start.41 = (f32[64,256]{1,0:T(8,128)S(1)}, f32[64,256]{1,0:T(8,128)S(1)}, u32[]{:S(2)}, u32[]{:S(2)}) collective-permute-start(f32[64,256]{1,0:T(8,128)S(1)} %get-tuple-element.75), channel_id=1, source_target_pairs={{0,2},{1,3},{2,0},{3,1},{4,6},{5,7},{6,4},{7,5},{8,10},{9,11},{10,... | collective-permute-start | bytes 196616 | tf_op jit(solution)/shard_map/ppermute | solution.py:33
  87.7 6.8 %collective-permute-start.39 = (f32[64,256]{1,0:T(8,128)S(1)}, f32[64,256]{1,0:T(8,128)S(1)}, u32[]{:S(2)}, u32[]{:S(2)}) collective-permute-start(f32[64,256]{1,0:T(8,128)S(1)} %get-tuple-element.75), channel_id=1, source_target_pairs={{0,1},{1,0},{2,3},{3,2},{4,5},{5,4},{6,7},{7,6},{8,9},{9,8},{10,11... | collective-permute-start | bytes 196616 | tf_op jit(solution)/shard_map/ppermute | solution.py:33
  89.8 8.3 %collective-permute-start.43 = (f32[64,256]{1,0:T(8,128)S(1)}, f32[64,256]{1,0:T(8,128)S(1)}, u32[]{:S(2)}, u32[]{:S(2)}) collective-permute-start(f32[64,256]{1,0:T(8,128)S(1)} %get-tuple-element.77.refs_6_), channel_id=1, source_target_pairs={{0,2},{1,3},{2,0},{3,1},{4,6},{5,7},{6,4},{7,5},{8,10},{9,11},{10,... | collective-permute-start | bytes 196616 | tf_op jit(solution)/shard_map/ppermute | solution.py:33
  91.4 7.3 %collective-permute-start.44 = (f32[64,256]{1,0:T(8,128)S(1)}, f32[64,256]{1,0:T(8,128)S(1)}, u32[]{:S(2)}, u32[]{:S(2)}) collective-permute-start(f32[64,256]{1,0:T(8,128)S(1)} %get-tuple-element.77.refs_6_), channel_id=1, source_target_pairs={{0,3},{1,2},{2,1},{3,0},{4,7},{5,6},{6,5},{7,4},{8,11},{9,10},{10,... | collective-permute-start | bytes 196616 | tf_op jit(solution)/shard_map/ppermute | solution.py:33
  92.9 5.8 %collective-permute-start.42 = (f32[64,256]{1,0:T(8,128)S(1)}, f32[64,256]{1,0:T(8,128)S(1)}, u32[]{:S(2)}, u32[]{:S(2)}) collective-permute-start(f32[64,256]{1,0:T(8,128)S(1)} %get-tuple-element.77.refs_6_), channel_id=1, source_target_pairs={{0,1},{1,0},{2,3},{3,2},{4,5},{5,4},{6,7},{7,6},{8,9},{9,8},{10,11... | collective-permute-start | bytes 196616 | tf_op jit(solution)/shard_map/ppermute | solution.py:33
  95.1 5.9 %collective-permute-start.46 = (f32[64,256]{1,0:T(8,128)S(1)}, f32[64,256]{1,0:T(8,128)S(1)}, u32[]{:S(2)}, u32[]{:S(2)}) collective-permute-start(f32[64,256]{1,0:T(8,128)S(1)} %get-tuple-element.79.refs_7_), channel_id=1, source_target_pairs={{0,2},{1,3},{2,0},{3,1},{4,6},{5,7},{6,4},{7,5},{8,10},{9,11},{10,... | collective-permute-start | bytes 196616 | tf_op jit(solution)/shard_map/ppermute | solution.py:33
  96.6 6.5 %collective-permute-start.47 = (f32[64,256]{1,0:T(8,128)S(1)}, f32[64,256]{1,0:T(8,128)S(1)}, u32[]{:S(2)}, u32[]{:S(2)}) collective-permute-start(f32[64,256]{1,0:T(8,128)S(1)} %get-tuple-element.79.refs_7_), channel_id=1, source_target_pairs={{0,3},{1,2},{2,1},{3,0},{4,7},{5,6},{6,5},{7,4},{8,11},{9,10},{10,... | collective-permute-start | bytes 196616 | tf_op jit(solution)/shard_map/ppermute | solution.py:33
  98.1 5.0 %collective-permute-start.45 = (f32[64,256]{1,0:T(8,128)S(1)}, f32[64,256]{1,0:T(8,128)S(1)}, u32[]{:S(2)}, u32[]{:S(2)}) collective-permute-start(f32[64,256]{1,0:T(8,128)S(1)} %get-tuple-element.79.refs_7_), channel_id=1, source_target_pairs={{0,1},{1,0},{2,3},{3,2},{4,5},{5,4},{6,7},{7,6},{8,9},{9,8},{10,11... | collective-permute-start | bytes 196616 | tf_op jit(solution)/shard_map/ppermute | solution.py:33
  104.4 1.4 %collective-permute-start.48 = (f32[4,16,512]{2,1,0:T(8,128)S(1)}, f32[4,16,512]{2,1,0:T(8,128)S(1)}, u32[]{:S(2)}, u32[]{:S(2)}) collective-permute-start(f32[4,16,512]{2,1,0:T(8,128)S(1)} %get-tuple-element.83), channel_id=1, source_target_pairs={{0,4},{4,0},{8,12},{12,8},{16,20},{20,16},{24,28},{28,24},{1,5},{5... | collective-permute-start | bytes 393224 | tf_op jit(solution)/shard_map/ppermute | solution.py:283
  105.8 5.3 %collective-permute-start.49 = (f32[2,16,512]{2,1,0:T(8,128)S(1)}, f32[2,16,512]{2,1,0:T(8,128)S(1)}, u32[]{:S(2)}, u32[]{:S(2)}) collective-permute-start(f32[2,16,512]{2,1,0:T(8,128)S(1)} %get-tuple-element.85), channel_id=1, source_target_pairs={{0,24},{4,28},{8,16},{12,20},{16,8},{20,12},{24,0},{28,4},{1,25},{... | collective-permute-start | bytes 196616 | tf_op jit(solution)/shard_map/ppermute | solution.py:83
  108.3 4.3 %collective-permute-start.50 = (f32[2,16,512]{2,1,0:T(8,128)S(1)}, f32[2,16,512]{2,1,0:T(8,128)S(1)}, u32[]{:S(2)}, u32[]{:S(2)}) collective-permute-start(f32[2,16,512]{2,1,0:T(8,128)S(1)} %get-tuple-element.86), channel_id=1, source_target_pairs={{0,16},{4,20},{8,24},{12,28},{16,0},{20,4},{24,8},{28,12},{1,17},{... | collective-permute-start | bytes 196616 | tf_op jit(solution)/shard_map/ppermute | solution.py:83
  108.8 4.3 %collective-permute-start.51 = (f32[2,16,512]{2,1,0:T(8,128)S(1)}, f32[2,16,512]{2,1,0:T(8,128)S(1)}, u32[]{:S(2)}, u32[]{:S(2)}) collective-permute-start(f32[2,16,512]{2,1,0:T(8,128)S(1)} %get-tuple-element.87), channel_id=1, source_target_pairs={{0,8},{4,12},{8,0},{12,4},{16,24},{20,28},{24,16},{28,20},{1,9},{5... | collective-permute-start | bytes 196616 | tf_op jit(solution)/shard_map/ppermute | solution.py:83
  113.5 5.7 %collective-permute-start.52 = (f32[16,1024]{1,0:T(8,128)S(1)}, f32[16,1024]{1,0:T(8,128)S(1)}, u32[]{:S(2)}, u32[]{:S(2)}) collective-permute-start(f32[16,1024]{1,0:T(8,128)S(1)} %get-tuple-element.89.refs_2_.refs_0_), channel_id=1, source_target_pairs={{0,2},{1,3},{2,0},{3,1},{4,6},{5,7},{6,4},{7,5},{8,10},{9,11},{10,... | collective-permute-start | bytes 196616 | tf_op jit(solution)/shard_map/ppermute | solution.py:33
  114.4 6.2 %collective-permute-start.53 = (f32[16,1024]{1,0:T(8,128)S(1)}, f32[16,1024]{1,0:T(8,128)S(1)}, u32[]{:S(2)}, u32[]{:S(2)}) collective-permute-start(f32[16,1024]{1,0:T(8,128)S(1)} %get-tuple-element.89.refs_2_.refs_0_), channel_id=1, source_target_pairs={{0,3},{1,2},{2,1},{3,0},{4,7},{5,6},{6,5},{7,4},{8,11},{9,10},{10,... | collective-permute-start | bytes 196616 | tf_op jit(solution)/shard_map/ppermute | solution.py:33
  115.9 5.0 %collective-permute-start.54 = (f32[16,1024]{1,0:T(8,128)S(1)}, f32[16,1024]{1,0:T(8,128)S(1)}, u32[]{:S(2)}, u32[]{:S(2)}) collective-permute-start(f32[16,1024]{1,0:T(8,128)S(1)} %get-tuple-element.89.refs_2_.refs_0_), channel_id=1, source_target_pairs={{0,1},{1,0},{2,3},{3,2},{4,5},{5,4},{6,7},{7,6},{8,9},{9,8},{10,11... | collective-permute-start | bytes 196616 | tf_op jit(solution)/shard_map/ppermute | solution.py:33
  121.2 5.1 %collective-permute-start.55 = (f32[16,512]{1,0:T(8,128)S(1)}, f32[16,512]{1,0:T(8,128)S(1)}, u32[]{:S(2)}, u32[]{:S(2)}) collective-permute-start(f32[16,512]{1,0:T(8,128)S(1)} %get-tuple-element.97), channel_id=1, source_target_pairs={{0,2},{1,3},{2,0},{3,1},{4,6},{5,7},{6,4},{7,5},{8,10},{9,11},{10,... | collective-permute-start | bytes 98312 | tf_op jit(solution)/shard_map/ppermute | solution.py:33
  122.4 5.9 %collective-permute-start.56 = (f32[16,512]{1,0:T(8,128)S(1)}, f32[16,512]{1,0:T(8,128)S(1)}, u32[]{:S(2)}, u32[]{:S(2)}) collective-permute-start(f32[16,512]{1,0:T(8,128)S(1)} %get-tuple-element.98), channel_id=1, source_target_pairs={{0,3},{1,2},{2,1},{3,0},{4,7},{5,6},{6,5},{7,4},{8,11},{9,10},{10,... | collective-permute-start | bytes 98312 | tf_op jit(solution)/shard_map/ppermute | solution.py:33
  124.1 4.3 %collective-permute-start.57 = (f32[16,512]{1,0:T(8,128)S(1)}, f32[16,512]{1,0:T(8,128)S(1)}, u32[]{:S(2)}, u32[]{:S(2)}) collective-permute-start(f32[16,512]{1,0:T(8,128)S(1)} %get-tuple-element.99), channel_id=1, source_target_pairs={{0,1},{1,0},{2,3},{3,2},{4,5},{5,4},{6,7},{7,6},{8,9},{9,8},{10,11... | collective-permute-start | bytes 98312 | tf_op jit(solution)/shard_map/ppermute | solution.py:33
  128.7 4.7 %collective-permute-start.58 = (f32[16,256]{1,0:T(8,128)S(1)}, f32[16,256]{1,0:T(8,128)S(1)}, u32[]{:S(2)}, u32[]{:S(2)}) collective-permute-start(f32[16,256]{1,0:T(8,128)S(1)} %shard_map.124.refs_0_), channel_id=1, source_target_pairs={{0,2},{1,3},{2,0},{3,1},{4,6},{5,7},{6,4},{7,5},{8,10},{9,11},{10,... | collective-permute-start | bytes 49160 | tf_op jit(solution)/shard_map/ppermute | solution.py:33
  129.7 5.5 %collective-permute-start.59 = (f32[16,256]{1,0:T(8,128)S(1)}, f32[16,256]{1,0:T(8,128)S(1)}, u32[]{:S(2)}, u32[]{:S(2)}) collective-permute-start(f32[16,256]{1,0:T(8,128)S(1)} %shard_map.124.refs_0_), channel_id=1, source_target_pairs={{0,3},{1,2},{2,1},{3,0},{4,7},{5,6},{6,5},{7,4},{8,11},{9,10},{10,... | collective-permute-start | bytes 49160 | tf_op jit(solution)/shard_map/ppermute | solution.py:33
  131.5 3.9 %collective-permute-start.60 = (f32[16,256]{1,0:T(8,128)S(1)}, f32[16,256]{1,0:T(8,128)S(1)}, u32[]{:S(2)}, u32[]{:S(2)}) collective-permute-start(f32[16,256]{1,0:T(8,128)S(1)} %shard_map.124.refs_0_), channel_id=1, source_target_pairs={{0,1},{1,0},{2,3},{3,2},{4,5},{5,4},{6,7},{7,6},{8,9},{9,8},{10,11... | collective-permute-start | bytes 49160 | tf_op jit(solution)/shard_map/ppermute | solution.py:33
  (7 other events, 87.6 us)

commit v25 on v22

--- a/solution.py
+++ b/solution.py
@@ -494,19 +494,19 @@
         for i in range(streams):
             turn_taken = step > 0 and last is not None
             ties = [(1, last[0][2][1])] if step * streams + i > streams else []
-            pieces = gather_rows(values[i], ties)
+            pieces = gather_rows(values[i], ties, step == 0)
             if step == 1 and i == 0:
                 later = turn(rhs_local, 1, supernodes, streams, pieces[1][1])
             if turn_taken:
                 offset, piece = pieces[2]
                 pieces[2] = (offset, lax.optimization_barrier((piece, last[1]))[0])
             if step == 0:
+                far_first, pieces = pieces, pieces[:1] + pieces[-1:] + pieces[1:-1]
                 owned = apply_split(
-                    [p for _, p in pieces],
+                    [p for _, p in far_first],
                     first_top,
                     first_rest,
                     0,
-                    far_first=False,
                 )
             else:
                 whole = assemble(pieces, order)

time: 134 us -> 135 us (level)
  transfers between devices with their start and end apart: 61 -> 61, of which waited for: 18 -> 21; matrix products, arithmetic and copies ran while one was open for 7% -> 7% of each run, Pallas kernels for 3% -> 3%
where the time goes in v25:
time: 135 us
  starting transfers between devices  91 us (67%)
  waiting for transfers between devices  23.3 us (17%)
  matrix products  7.53 us (6%)
  Pallas kernels  7.52 us (6%)
  between operations  2.03 us (2%)
  local copies, waits for them, and re-layouts  1.83 us (1%)
  other arithmetic  1.41 us (1%)
    ppermute x57, starting transfers between devices, send(): return lax.ppermute(value, axis, pairs)  87.4 us
    ppermute x57, waiting for transfers between devices, send(): return lax.ppermute(value, axis, pairs)  19.2 us
    dot_general x12, matrix products, contract_last(): lax.dot_general(left, right, (((left.ndim - 1,), (right.ndim - 1,)), ((),...  7.53 us
    pallas_call x13, Pallas kernels, local_kernel(): pl.pallas_call(body, out_shape=list(outs), in_specs=specs or [VMEM] * len...  7.52 us
    ppermute x3, starting transfers between devices, swap(): return lax.ppermute(value, axis, pairs)  3.55 us
    ppermute x3, waiting for transfers between devices, swap(): return lax.ppermute(value, axis, pairs)  2.73 us
  transfers between devices with their start and end apart: 61, of which 21 were waited for; matrix products, arithmetic and copies ran while one was open for 7% of the time, Pallas kernels for 3%

profile of v25, /device:TPU:0, one launch (start us, length us, event | category | flops | bytes accessed | tf_op | source)
XLA Modules:
  0.0 134.6 jit_solution(10744751360480766674)
XLA Ops:
  0.6 1.0 copy-done.2
  1.9 4.1 %collective-permute-start = (f32[64,256]{1,0:T(8,128)S(1)}, f32[64,256]{1,0:T(8,128)S(1)}, u32[]{:S(2)}, u32[]{:S(2)}) collective-permute-start(f32[64,256]{1,0:T(8,128)S(1)} %get-tuple-element.52.refs_0_), channel_id=1, source_target_pairs={{0,2},{1,3},{2,0},{3,1},{4,6},{5,7},{6,4},{7,5},{8,10},{9,11},{10,... | collective-permute-start | bytes 196616 | tf_op jit(solution)/shard_map/ppermute | solution.py:33
  6.0 1.3 %collective-permute-start.1 = (f32[64,256]{1,0:T(8,128)S(1)}, f32[64,256]{1,0:T(8,128)S(1)}, u32[]{:S(2)}, u32[]{:S(2)}) collective-permute-start(f32[64,256]{1,0:T(8,128)S(1)} %get-tuple-element.52.refs_0_), channel_id=1, source_target_pairs={{0,3},{1,2},{2,1},{3,0},{4,7},{5,6},{6,5},{7,4},{8,11},{9,10},{10,... | collective-permute-start | bytes 196616 | tf_op jit(solution)/shard_map/ppermute | solution.py:33
  7.6 2.8 %collective-permute-start.3 = (f32[64,256]{1,0:T(8,128)S(1)}, f32[64,256]{1,0:T(8,128)S(1)}, u32[]{:S(2)}, u32[]{:S(2)}) collective-permute-start(f32[64,256]{1,0:T(8,128)S(1)} %get-tuple-element.53.refs_0_), channel_id=1, source_target_pairs={{0,2},{1,3},{2,0},{3,1},{4,6},{5,7},{6,4},{7,5},{8,10},{9,11},{10,... | collective-permute-start | bytes 196616 | tf_op jit(solution)/shard_map/ppermute | solution.py:33
  10.4 1.3 %collective-permute-start.4 = (f32[64,256]{1,0:T(8,128)S(1)}, f32[64,256]{1,0:T(8,128)S(1)}, u32[]{:S(2)}, u32[]{:S(2)}) collective-permute-start(f32[64,256]{1,0:T(8,128)S(1)} %get-tuple-element.53.refs_0_), channel_id=1, source_target_pairs={{0,3},{1,2},{2,1},{3,0},{4,7},{5,6},{6,5},{7,4},{8,11},{9,10},{10,... | collective-permute-start | bytes 196616 | tf_op jit(solution)/shard_map/ppermute | solution.py:33
  11.8 0.6 collective-permute-start.5
  12.4 1.4 %fusion = (bf16[1,256,1024]{2,1,0:T(8,128)(2,1)S(1)}, bf16[1,256,1024]{2,1,0:T(8,128)(2,1)S(1)}) fusion(f32[1,4,256,1024]{3,2,1,0:T(8,128)} %param.11), kind=kLoop, calls=%fused_computation.2 | loop fusion | flops 1048576 | bytes 2097152 | tf_op jit(solution)/shard_map/convert_element_type | solution.py:487
  15.0 1.7 %collective-permute-start.6 = (f32[64,256]{1,0:T(8,128)S(1)}, f32[64,256]{1,0:T(8,128)S(1)}, u32[]{:S(2)}, u32[]{:S(2)}) collective-permute-start(f32[64,256]{1,0:T(8,128)S(1)} %shard_map.114.refs_0_), channel_id=1, source_target_pairs={{0,1},{1,0},{2,3},{3,2},{4,5},{5,4},{6,7},{7,6},{8,9},{9,8},{10,11... | collective-permute-start | bytes 196616 | tf_op jit(solution)/shard_map/ppermute | solution.py:33
  16.7 3.4 %collective-permute-start.7 = (f32[64,256]{1,0:T(8,128)S(1)}, f32[64,256]{1,0:T(8,128)S(1)}, u32[]{:S(2)}, u32[]{:S(2)}) collective-permute-start(f32[64,256]{1,0:T(8,128)S(1)} %shard_map.114.refs_0_), channel_id=1, source_target_pairs={{0,2},{1,3},{2,0},{3,1},{4,6},{5,7},{6,4},{7,5},{8,10},{9,11},{10,... | collective-permute-start | bytes 196616 | tf_op jit(solution)/shard_map/ppermute | solution.py:33
  20.1 1.4 %collective-permute-start.8 = (f32[64,256]{1,0:T(8,128)S(1)}, f32[64,256]{1,0:T(8,128)S(1)}, u32[]{:S(2)}, u32[]{:S(2)}) collective-permute-start(f32[64,256]{1,0:T(8,128)S(1)} %shard_map.114.refs_0_), channel_id=1, source_target_pairs={{0,3},{1,2},{2,1},{3,0},{4,7},{5,6},{6,5},{7,4},{8,11},{9,10},{10,... | collective-permute-start | bytes 196616 | tf_op jit(solution)/shard_map/ppermute | solution.py:33
  21.9 2.1 %collective-permute-start.9 = (f32[64,256]{1,0:T(8,128)S(1)}, f32[64,256]{1,0:T(8,128)S(1)}, u32[]{:S(2)}, u32[]{:S(2)}) collective-permute-start(f32[64,256]{1,0:T(8,128)S(1)} %shard_map.115.refs_1_), channel_id=1, source_target_pairs={{0,2},{1,3},{2,0},{3,1},{4,6},{5,7},{6,4},{7,5},{8,10},{9,11},{10,... | collective-permute-start | bytes 196616 | tf_op jit(solution)/shard_map/ppermute | solution.py:33
  24.0 0.9 collective-permute-start.13
  25.0 1.2 collective-permute-done.7
  27.9 6.3 %collective-permute-start.11 = (f32[64,256]{1,0:T(8,128)S(1)}, f32[64,256]{1,0:T(8,128)S(1)}, u32[]{:S(2)}, u32[]{:S(2)}) collective-permute-start(f32[64,256]{1,0:T(8,128)S(1)} %get-tuple-element.56), channel_id=1, source_target_pairs={{0,2},{1,3},{2,0},{3,1},{4,6},{5,7},{6,4},{7,5},{8,10},{9,11},{10,... | collective-permute-start | bytes 196616 | tf_op jit(solution)/shard_map/ppermute | solution.py:33
  34.2 0.6 collective-permute-start.10
  34.9 0.6 constant_dynamic-update-slice_fusion.43
  35.5 3.8 %collective-permute-start.16 = (f32[64,256]{1,0:T(8,128)S(1)}, f32[64,256]{1,0:T(8,128)S(1)}, u32[]{:S(2)}, u32[]{:S(2)}) collective-permute-start(f32[64,256]{1,0:T(8,128)S(1)} %get-tuple-element.59), channel_id=1, source_target_pairs={{0,2},{1,3},{2,0},{3,1},{4,6},{5,7},{6,4},{7,5},{8,10},{9,11},{10,... | collective-permute-start | bytes 196616 | tf_op jit(solution)/shard_map/ppermute | solution.py:33
  39.3 0.6 collective-permute-start.15
  40.0 1.1 collective-permute-done.10
  41.8 2.7 %collective-permute-start.19 = (f32[64,256]{1,0:T(8,128)S(1)}, f32[64,256]{1,0:T(8,128)S(1)}, u32[]{:S(2)}, u32[]{:S(2)}) collective-permute-start(f32[64,256]{1,0:T(8,128)S(1)} %get-tuple-element.61.refs_2_), channel_id=1, source_target_pairs={{0,2},{1,3},{2,0},{3,1},{4,6},{5,7},{6,4},{7,5},{8,10},{9,11},{10,... | collective-permute-start | bytes 196616 | tf_op jit(solution)/shard_map/ppermute | solution.py:33
  44.6 0.8 collective-permute-start.18
  46.4 3.3 %collective-permute-start.21 = (f32[64,256]{1,0:T(8,128)S(1)}, f32[64,256]{1,0:T(8,128)S(1)}, u32[]{:S(2)}, u32[]{:S(2)}) collective-permute-start(f32[64,256]{1,0:T(8,128)S(1)} %get-tuple-element.65.refs_3_), channel_id=1, source_target_pairs={{0,2},{1,3},{2,0},{3,1},{4,6},{5,7},{6,4},{7,5},{8,10},{9,11},{10,... | collective-permute-start | bytes 196616 | tf_op jit(solution)/shard_map/ppermute | solution.py:33
  50.2 0.8 collective-permute-start.24
  51.7 4.9 %collective-permute-start.23 = (f32[64,256]{1,0:T(8,128)S(1)}, f32[64,256]{1,0:T(8,128)S(1)}, u32[]{:S(2)}, u32[]{:S(2)}) collective-permute-start(f32[64,256]{1,0:T(8,128)S(1)} %get-tuple-element.64), channel_id=1, source_target_pairs={{0,2},{1,3},{2,0},{3,1},{4,6},{5,7},{6,4},{7,5},{8,10},{9,11},{10,... | collective-permute-start | bytes 196616 | tf_op jit(solution)/shard_map/ppermute | solution.py:33
  57.9 3.8 %collective-permute-start.28 = (f32[64,256]{1,0:T(8,128)S(1)}, f32[64,256]{1,0:T(8,128)S(1)}, u32[]{:S(2)}, u32[]{:S(2)}) collective-permute-start(f32[64,256]{1,0:T(8,128)S(1)} %get-tuple-element.67), channel_id=1, source_target_pairs={{0,2},{1,3},{2,0},{3,1},{4,6},{5,7},{6,4},{7,5},{8,10},{9,11},{10,... | collective-permute-start | bytes 196616 | tf_op jit(solution)/shard_map/ppermute | solution.py:33
  63.5 3.4 %collective-permute-start.31 = (f32[64,256]{1,0:T(8,128)S(1)}, f32[64,256]{1,0:T(8,128)S(1)}, u32[]{:S(2)}, u32[]{:S(2)}) collective-permute-start(f32[64,256]{1,0:T(8,128)S(1)} %get-tuple-element.69.refs_4_), channel_id=1, source_target_pairs={{0,2},{1,3},{2,0},{3,1},{4,6},{5,7},{6,4},{7,5},{8,10},{9,11},{10,... | collective-permute-start | bytes 196616 | tf_op jit(solution)/shard_map/ppermute | solution.py:33
  66.9 0.9 collective-permute-start.32
  68.7 3.5 %collective-permute-start.33 = (f32[64,256]{1,0:T(8,128)S(1)}, f32[64,256]{1,0:T(8,128)S(1)}, u32[]{:S(2)}, u32[]{:S(2)}) collective-permute-start(f32[64,256]{1,0:T(8,128)S(1)} %get-tuple-element.73.refs_5_), channel_id=1, source_target_pairs={{0,2},{1,3},{2,0},{3,1},{4,6},{5,7},{6,4},{7,5},{8,10},{9,11},{10,... | collective-permute-start | bytes 196616 | tf_op jit(solution)/shard_map/ppermute | solution.py:33
  72.1 1.8 %collective-permute-start.37 = (f32[64,256]{1,0:T(8,128)S(1)}, f32[64,256]{1,0:T(8,128)S(1)}, u32[]{:S(2)}, u32[]{:S(2)}) collective-permute-start(f32[64,256]{1,0:T(8,128)S(1)} %get-tuple-element.73.refs_5_), channel_id=1, source_target_pairs={{0,3},{1,2},{2,1},{3,0},{4,7},{5,6},{6,5},{7,4},{8,11},{9,10},{10,... | collective-permute-start | bytes 196616 | tf_op jit(solution)/shard_map/ppermute | solution.py:33
  74.7 3.7 %collective-permute-start.35 = (f32[64,256]{1,0:T(8,128)S(1)}, f32[64,256]{1,0:T(8,128)S(1)}, u32[]{:S(2)}, u32[]{:S(2)}) collective-permute-start(f32[64,256]{1,0:T(8,128)S(1)} %get-tuple-element.72), channel_id=1, source_target_pairs={{0,2},{1,3},{2,0},{3,1},{4,6},{5,7},{6,4},{7,5},{8,10},{9,11},{10,... | collective-permute-start | bytes 196616 | tf_op jit(solution)/shard_map/ppermute | solution.py:33
  78.3 0.8 collective-permute-start.38
  79.1 0.7 collective-permute-done.36
  80.6 3.0 %collective-permute-start.40 = (f32[64,256]{1,0:T(8,128)S(1)}, f32[64,256]{1,0:T(8,128)S(1)}, u32[]{:S(2)}, u32[]{:S(2)}) collective-permute-start(f32[64,256]{1,0:T(8,128)S(1)} %get-tuple-element.75), channel_id=1, source_target_pairs={{0,2},{1,3},{2,0},{3,1},{4,6},{5,7},{6,4},{7,5},{8,10},{9,11},{10,... | collective-permute-start | bytes 196616 | tf_op jit(solution)/shard_map/ppermute | solution.py:33
  83.5 1.6 %collective-permute-start.41 = (f32[64,256]{1,0:T(8,128)S(1)}, f32[64,256]{1,0:T(8,128)S(1)}, u32[]{:S(2)}, u32[]{:S(2)}) collective-permute-start(f32[64,256]{1,0:T(8,128)S(1)} %get-tuple-element.75), channel_id=1, source_target_pairs={{0,3},{1,2},{2,1},{3,0},{4,7},{5,6},{6,5},{7,4},{8,11},{9,10},{10,... | collective-permute-start | bytes 196616 | tf_op jit(solution)/shard_map/ppermute | solution.py:33
  85.9 3.7 %collective-permute-start.43 = (f32[64,256]{1,0:T(8,128)S(1)}, f32[64,256]{1,0:T(8,128)S(1)}, u32[]{:S(2)}, u32[]{:S(2)}) collective-permute-start(f32[64,256]{1,0:T(8,128)S(1)} %get-tuple-element.77.refs_6_), channel_id=1, source_target_pairs={{0,2},{1,3},{2,0},{3,1},{4,6},{5,7},{6,4},{7,5},{8,10},{9,11},{10,... | collective-permute-start | bytes 196616 | tf_op jit(solution)/shard_map/ppermute | solution.py:33
  89.6 0.8 collective-permute-start.44
  90.4 1.6 %collective-permute-done.39 = f32[64,256]{1,0:T(8,128)S(1)} collective-permute-done((f32[64,256]{1,0:T(8,128)S(1)}, f32[64,256]{1,0:T(8,128)S(1)}, u32[]{:S(2)}, u32[]{:S(2)}) %collective-permute-start.39) | collective-permute-done | bytes 65568 | tf_op jit(solution)/shard_map/ppermute | solution.py:33
  92.7 2.1 %collective-permute-start.46 = (f32[64,256]{1,0:T(8,128)S(1)}, f32[64,256]{1,0:T(8,128)S(1)}, u32[]{:S(2)}, u32[]{:S(2)}) collective-permute-start(f32[64,256]{1,0:T(8,128)S(1)} %get-tuple-element.79.refs_7_), channel_id=1, source_target_pairs={{0,2},{1,3},{2,0},{3,1},{4,6},{5,7},{6,4},{7,5},{8,10},{9,11},{10,... | collective-permute-start | bytes 196616 | tf_op jit(solution)/shard_map/ppermute | solution.py:33
  94.8 1.6 %collective-permute-start.47 = (f32[64,256]{1,0:T(8,128)S(1)}, f32[64,256]{1,0:T(8,128)S(1)}, u32[]{:S(2)}, u32[]{:S(2)}) collective-permute-start(f32[64,256]{1,0:T(8,128)S(1)} %get-tuple-element.79.refs_7_), channel_id=1, source_target_pairs={{0,3},{1,2},{2,1},{3,0},{4,7},{5,6},{6,5},{7,4},{8,11},{9,10},{10,... | collective-permute-start | bytes 196616 | tf_op jit(solution)/shard_map/ppermute | solution.py:33
  96.4 1.5 %collective-permute-done.46 = f32[64,256]{1,0:T(8,128)S(1)} collective-permute-done((f32[64,256]{1,0:T(8,128)S(1)}, f32[64,256]{1,0:T(8,128)S(1)}, u32[]{:S(2)}, u32[]{:S(2)}) %collective-permute-start.46) | collective-permute-done | bytes 65568 | tf_op jit(solution)/shard_map/ppermute | solution.py:33
  98.0 1.2 shard_map.117.refs_0_
  99.1 2.2 %collective-permute-done.45 = f32[64,256]{1,0:T(8,128)S(1)} collective-permute-done((f32[64,256]{1,0:T(8,128)S(1)}, f32[64,256]{1,0:T(8,128)S(1)}, u32[]{:S(2)}, u32[]{:S(2)}) %collective-permute-start.45) | collective-permute-done | bytes 65568 | tf_op jit(solution)/shard_map/ppermute | solution.py:33
  101.4 1.2 shard_map.118
  102.7 1.3 collective-permute-done.48.refs_1_
  104.1 2.5 %collective-permute-start.49 = (f32[2,16,512]{2,1,0:T(8,128)S(1)}, f32[2,16,512]{2,1,0:T(8,128)S(1)}, u32[]{:S(2)}, u32[]{:S(2)}) collective-permute-start(f32[2,16,512]{2,1,0:T(8,128)S(1)} %get-tuple-element.85), channel_id=1, source_target_pairs={{0,24},{4,28},{8,16},{12,20},{16,8},{20,12},{24,0},{28,4},{1,25},{... | collective-permute-start | bytes 196616 | tf_op jit(solution)/shard_map/ppermute | solution.py:81
  107.6 1.0 shard_map.119
  108.6 0.7 collective-permute-done.49.refs_1_
  109.3 1.5 %collective-permute-done.50.refs_2_ = f32[2,16,512]{2,1,0:T(8,128)S(1)} collective-permute-done((f32[2,16,512]{2,1,0:T(8,128)S(1)}, f32[2,16,512]{2,1,0:T(8,128)S(1)}, u32[]{:S(2)}, u32[]{:S(2)}) %collective-permute-start.50) | collective-permute-done | bytes 65568 | tf_op jit(solution)/shard_map/ppermute | solution.py:81
  111.7 0.8 collective-permute-start.52
  112.6 1.6 %collective-permute-start.53 = (f32[16,1024]{1,0:T(8,128)S(1)}, f32[16,1024]{1,0:T(8,128)S(1)}, u32[]{:S(2)}, u32[]{:S(2)}) collective-permute-start(f32[16,1024]{1,0:T(8,128)S(1)} %get-tuple-element.89.refs_2_.refs_0_), channel_id=1, source_target_pairs={{0,3},{1,2},{2,1},{3,0},{4,7},{5,6},{6,5},{7,4},{8,11},{9,10},{10,... | collective-permute-start | bytes 196616 | tf_op jit(solution)/shard_map/ppermute | solution.py:33
  114.2 1.1 collective-permute-start.54
  115.8 1.7 %collective-permute-done.52.refs_1_ = f32[16,1024]{1,0:T(8,128)S(1)} collective-permute-done((f32[16,1024]{1,0:T(8,128)S(1)}, f32[16,1024]{1,0:T(8,128)S(1)}, u32[]{:S(2)}, u32[]{:S(2)}) %collective-permute-start.52) | collective-permute-done | bytes 65568 | tf_op jit(solution)/shard_map/ppermute | solution.py:33
  117.5 1.3 collective-permute-done.53.refs_2_
  119.5 1.1 collective-permute-start.55
  120.6 1.7 %collective-permute-start.56 = (f32[16,512]{1,0:T(8,128)S(1)}, f32[16,512]{1,0:T(8,128)S(1)}, u32[]{:S(2)}, u32[]{:S(2)}) collective-permute-start(f32[16,512]{1,0:T(8,128)S(1)} %get-tuple-element.98), channel_id=1, source_target_pairs={{0,3},{1,2},{2,1},{3,0},{4,7},{5,6},{6,5},{7,4},{8,11},{9,10},{10,... | collective-permute-start | bytes 98312 | tf_op jit(solution)/shard_map/ppermute | solution.py:33
  122.3 0.7 collective-permute-start.57
  123.0 1.5 %collective-permute-done.55.refs_2_ = f32[16,512]{1,0:T(8,128)S(1)} collective-permute-done((f32[16,512]{1,0:T(8,128)S(1)}, f32[16,512]{1,0:T(8,128)S(1)}, u32[]{:S(2)}, u32[]{:S(2)}) %collective-permute-start.55) | collective-permute-done | bytes 32800 | tf_op jit(solution)/shard_map/ppermute | solution.py:33
  124.6 1.9 %collective-permute-done.56.refs_3_ = f32[16,512]{1,0:T(8,128)S(1)} collective-permute-done((f32[16,512]{1,0:T(8,128)S(1)}, f32[16,512]{1,0:T(8,128)S(1)}, u32[]{:S(2)}, u32[]{:S(2)}) %collective-permute-start.56) | collective-permute-done | bytes 32800 | tf_op jit(solution)/shard_map/ppermute | solution.py:33
  127.0 0.9 collective-permute-start.58
  127.9 1.9 %collective-permute-start.59 = (f32[16,256]{1,0:T(8,128)S(1)}, f32[16,256]{1,0:T(8,128)S(1)}, u32[]{:S(2)}, u32[]{:S(2)}) collective-permute-start(f32[16,256]{1,0:T(8,128)S(1)} %shard_map.124.refs_0_), channel_id=1, source_target_pairs={{0,3},{1,2},{2,1},{3,0},{4,7},{5,6},{6,5},{7,4},{8,11},{9,10},{10,... | collective-permute-start | bytes 49160 | tf_op jit(solution)/shard_map/ppermute | solution.py:33
  129.8 0.7 collective-permute-start.60
  130.5 1.2 collective-permute-done.58.refs_1_
  131.7 1.8 %collective-permute-done.59.refs_2_ = f32[16,256]{1,0:T(8,128)S(1)} collective-permute-done((f32[16,256]{1,0:T(8,128)S(1)}, f32[16,256]{1,0:T(8,128)S(1)}, u32[]{:S(2)}, u32[]{:S(2)}) %collective-permute-start.59) | collective-permute-done | bytes 16416 | tf_op jit(solution)/shard_map/ppermute | solution.py:33
  133.6 1.0 shard_map.125
  (162 shorter events, 16.5 us)
Async XLA Ops:
  1.7 25.1 %copy-start.3 = (f32[1,4,256,128]{3,2,1,0:T(8,128)S(1)}, f32[1,4,256,128]{3,2,1,0:T(8,128)}, u32[]{:S(2)}) copy-start(f32[1,4,256,128]{3,2,1,0:T(8,128)} %rhs_ref.3) | copy-start | bytes 1572868
  1.9 9.8 %collective-permute-start = (f32[64,256]{1,0:T(8,128)S(1)}, f32[64,256]{1,0:T(8,128)S(1)}, u32[]{:S(2)}, u32[]{:S(2)}) collective-permute-start(f32[64,256]{1,0:T(8,128)S(1)} %get-tuple-element.52.refs_0_), channel_id=1, source_target_pairs={{0,2},{1,3},{2,0},{3,1},{4,6},{5,7},{6,4},{7,5},{8,10},{9,11},{10,... | collective-permute-start | bytes 196616 | tf_op jit(solution)/shard_map/ppermute | solution.py:33
  6.0 8.5 %collective-permute-start.1 = (f32[64,256]{1,0:T(8,128)S(1)}, f32[64,256]{1,0:T(8,128)S(1)}, u32[]{:S(2)}, u32[]{:S(2)}) collective-permute-start(f32[64,256]{1,0:T(8,128)S(1)} %get-tuple-element.52.refs_0_), channel_id=1, source_target_pairs={{0,3},{1,2},{2,1},{3,0},{4,7},{5,6},{6,5},{7,4},{8,11},{9,10},{10,... | collective-permute-start | bytes 196616 | tf_op jit(solution)/shard_map/ppermute | solution.py:33
  7.4 7.1 %collective-permute-start.2 = (f32[64,256]{1,0:T(8,128)S(1)}, f32[64,256]{1,0:T(8,128)S(1)}, u32[]{:S(2)}, u32[]{:S(2)}) collective-permute-start(f32[64,256]{1,0:T(8,128)S(1)} %get-tuple-element.52.refs_0_), channel_id=1, source_target_pairs={{0,1},{1,0},{2,3},{3,2},{4,5},{5,4},{6,7},{7,6},{8,9},{9,8},{10,11... | collective-permute-start | bytes 196616 | tf_op jit(solution)/shard_map/ppermute | solution.py:33
  7.6 12.5 %collective-permute-start.3 = (f32[64,256]{1,0:T(8,128)S(1)}, f32[64,256]{1,0:T(8,128)S(1)}, u32[]{:S(2)}, u32[]{:S(2)}) collective-permute-start(f32[64,256]{1,0:T(8,128)S(1)} %get-tuple-element.53.refs_0_), channel_id=1, source_target_pairs={{0,2},{1,3},{2,0},{3,1},{4,6},{5,7},{6,4},{7,5},{8,10},{9,11},{10,... | collective-permute-start | bytes 196616 | tf_op jit(solution)/shard_map/ppermute | solution.py:33
  10.4 11.0 %collective-permute-start.4 = (f32[64,256]{1,0:T(8,128)S(1)}, f32[64,256]{1,0:T(8,128)S(1)}, u32[]{:S(2)}, u32[]{:S(2)}) collective-permute-start(f32[64,256]{1,0:T(8,128)S(1)} %get-tuple-element.53.refs_0_), channel_id=1, source_target_pairs={{0,3},{1,2},{2,1},{3,0},{4,7},{5,6},{6,5},{7,4},{8,11},{9,10},{10,... | collective-permute-start | bytes 196616 | tf_op jit(solution)/shard_map/ppermute | solution.py:33
  11.8 9.7 %collective-permute-start.5 = (f32[64,256]{1,0:T(8,128)S(1)}, f32[64,256]{1,0:T(8,128)S(1)}, u32[]{:S(2)}, u32[]{:S(2)}) collective-permute-start(f32[64,256]{1,0:T(8,128)S(1)} %get-tuple-element.53.refs_0_), channel_id=1, source_target_pairs={{0,1},{1,0},{2,3},{3,2},{4,5},{5,4},{6,7},{7,6},{8,9},{9,8},{10,11... | collective-permute-start | bytes 196616 | tf_op jit(solution)/shard_map/ppermute | solution.py:33
  15.0 11.8 %collective-permute-start.6 = (f32[64,256]{1,0:T(8,128)S(1)}, f32[64,256]{1,0:T(8,128)S(1)}, u32[]{:S(2)}, u32[]{:S(2)}) collective-permute-start(f32[64,256]{1,0:T(8,128)S(1)} %shard_map.114.refs_0_), channel_id=1, source_target_pairs={{0,1},{1,0},{2,3},{3,2},{4,5},{5,4},{6,7},{7,6},{8,9},{9,8},{10,11... | collective-permute-start | bytes 196616 | tf_op jit(solution)/shard_map/ppermute | solution.py:33
  16.7 9.6 %collective-permute-start.7 = (f32[64,256]{1,0:T(8,128)S(1)}, f32[64,256]{1,0:T(8,128)S(1)}, u32[]{:S(2)}, u32[]{:S(2)}) collective-permute-start(f32[64,256]{1,0:T(8,128)S(1)} %shard_map.114.refs_0_), channel_id=1, source_target_pairs={{0,2},{1,3},{2,0},{3,1},{4,6},{5,7},{6,4},{7,5},{8,10},{9,11},{10,... | collective-permute-start | bytes 196616 | tf_op jit(solution)/shard_map/ppermute | solution.py:33
  20.1 7.1 %collective-permute-start.8 = (f32[64,256]{1,0:T(8,128)S(1)}, f32[64,256]{1,0:T(8,128)S(1)}, u32[]{:S(2)}, u32[]{:S(2)}) collective-permute-start(f32[64,256]{1,0:T(8,128)S(1)} %shard_map.114.refs_0_), channel_id=1, source_target_pairs={{0,3},{1,2},{2,1},{3,0},{4,7},{5,6},{6,5},{7,4},{8,11},{9,10},{10,... | collective-permute-start | bytes 196616 | tf_op jit(solution)/shard_map/ppermute | solution.py:33
  21.9 12.2 %collective-permute-start.9 = (f32[64,256]{1,0:T(8,128)S(1)}, f32[64,256]{1,0:T(8,128)S(1)}, u32[]{:S(2)}, u32[]{:S(2)}) collective-permute-start(f32[64,256]{1,0:T(8,128)S(1)} %shard_map.115.refs_1_), channel_id=1, source_target_pairs={{0,2},{1,3},{2,0},{3,1},{4,6},{5,7},{6,4},{7,5},{8,10},{9,11},{10,... | collective-permute-start | bytes 196616 | tf_op jit(solution)/shard_map/ppermute | solution.py:33
  24.0 10.8 %collective-permute-start.13 = (f32[64,256]{1,0:T(8,128)S(1)}, f32[64,256]{1,0:T(8,128)S(1)}, u32[]{:S(2)}, u32[]{:S(2)}) collective-permute-start(f32[64,256]{1,0:T(8,128)S(1)} %shard_map.115.refs_1_), channel_id=1, source_target_pairs={{0,3},{1,2},{2,1},{3,0},{4,7},{5,6},{6,5},{7,4},{8,11},{9,10},{10,... | collective-permute-start | bytes 196616 | tf_op jit(solution)/shard_map/ppermute | solution.py:33
  26.3 8.5 %collective-permute-start.12 = (f32[64,256]{1,0:T(8,128)S(1)}, f32[64,256]{1,0:T(8,128)S(1)}, u32[]{:S(2)}, u32[]{:S(2)}) collective-permute-start(f32[64,256]{1,0:T(8,128)S(1)} %shard_map.115.refs_1_), channel_id=1, source_target_pairs={{0,1},{1,0},{2,3},{3,2},{4,5},{5,4},{6,7},{7,6},{8,9},{9,8},{10,11... | collective-permute-start | bytes 196616 | tf_op jit(solution)/shard_map/ppermute | solution.py:33
  27.9 11.5 %collective-permute-start.11 = (f32[64,256]{1,0:T(8,128)S(1)}, f32[64,256]{1,0:T(8,128)S(1)}, u32[]{:S(2)}, u32[]{:S(2)}) collective-permute-start(f32[64,256]{1,0:T(8,128)S(1)} %get-tuple-element.56), channel_id=1, source_target_pairs={{0,2},{1,3},{2,0},{3,1},{4,6},{5,7},{6,4},{7,5},{8,10},{9,11},{10,... | collective-permute-start | bytes 196616 | tf_op jit(solution)/shard_map/ppermute | solution.py:33
  34.2 7.0 %collective-permute-start.14 = (f32[64,256]{1,0:T(8,128)S(1)}, f32[64,256]{1,0:T(8,128)S(1)}, u32[]{:S(2)}, u32[]{:S(2)}) collective-permute-start(f32[64,256]{1,0:T(8,128)S(1)} %get-tuple-element.56), channel_id=1, source_target_pairs={{0,3},{1,2},{2,1},{3,0},{4,7},{5,6},{6,5},{7,4},{8,11},{9,10},{10,... | collective-permute-start | bytes 196616 | tf_op jit(solution)/shard_map/ppermute | solution.py:33
  34.2 6.9 %collective-permute-start.10 = (f32[64,256]{1,0:T(8,128)S(1)}, f32[64,256]{1,0:T(8,128)S(1)}, u32[]{:S(2)}, u32[]{:S(2)}) collective-permute-start(f32[64,256]{1,0:T(8,128)S(1)} %get-tuple-element.56), channel_id=1, source_target_pairs={{0,1},{1,0},{2,3},{3,2},{4,5},{5,4},{6,7},{7,6},{8,9},{9,8},{10,11... | collective-permute-start | bytes 196616 | tf_op jit(solution)/shard_map/ppermute | solution.py:33
  35.5 9.0 %collective-permute-start.16 = (f32[64,256]{1,0:T(8,128)S(1)}, f32[64,256]{1,0:T(8,128)S(1)}, u32[]{:S(2)}, u32[]{:S(2)}) collective-permute-start(f32[64,256]{1,0:T(8,128)S(1)} %get-tuple-element.59), channel_id=1, source_target_pairs={{0,2},{1,3},{2,0},{3,1},{4,6},{5,7},{6,4},{7,5},{8,10},{9,11},{10,... | collective-permute-start | bytes 196616 | tf_op jit(solution)/shard_map/ppermute | solution.py:33
  39.3 6.4 %collective-permute-start.17 = (f32[64,256]{1,0:T(8,128)S(1)}, f32[64,256]{1,0:T(8,128)S(1)}, u32[]{:S(2)}, u32[]{:S(2)}) collective-permute-start(f32[64,256]{1,0:T(8,128)S(1)} %get-tuple-element.59), channel_id=1, source_target_pairs={{0,3},{1,2},{2,1},{3,0},{4,7},{5,6},{6,5},{7,4},{8,11},{9,10},{10,... | collective-permute-start | bytes 196616 | tf_op jit(solution)/shard_map/ppermute | solution.py:33
  39.3 6.0 %collective-permute-start.15 = (f32[64,256]{1,0:T(8,128)S(1)}, f32[64,256]{1,0:T(8,128)S(1)}, u32[]{:S(2)}, u32[]{:S(2)}) collective-permute-start(f32[64,256]{1,0:T(8,128)S(1)} %get-tuple-element.59), channel_id=1, source_target_pairs={{0,1},{1,0},{2,3},{3,2},{4,5},{5,4},{6,7},{7,6},{8,9},{9,8},{10,11... | collective-permute-start | bytes 196616 | tf_op jit(solution)/shard_map/ppermute | solution.py:33
  41.8 8.4 %collective-permute-start.19 = (f32[64,256]{1,0:T(8,128)S(1)}, f32[64,256]{1,0:T(8,128)S(1)}, u32[]{:S(2)}, u32[]{:S(2)}) collective-permute-start(f32[64,256]{1,0:T(8,128)S(1)} %get-tuple-element.61.refs_2_), channel_id=1, source_target_pairs={{0,2},{1,3},{2,0},{3,1},{4,6},{5,7},{6,4},{7,5},{8,10},{9,11},{10,... | collective-permute-start | bytes 196616 | tf_op jit(solution)/shard_map/ppermute | solution.py:33
  44.5 6.5 %collective-permute-start.20 = (f32[64,256]{1,0:T(8,128)S(1)}, f32[64,256]{1,0:T(8,128)S(1)}, u32[]{:S(2)}, u32[]{:S(2)}) collective-permute-start(f32[64,256]{1,0:T(8,128)S(1)} %get-tuple-element.61.refs_2_), channel_id=1, source_target_pairs={{0,3},{1,2},{2,1},{3,0},{4,7},{5,6},{6,5},{7,4},{8,11},{9,10},{10,... | collective-permute-start | bytes 196616 | tf_op jit(solution)/shard_map/ppermute | solution.py:33
  44.6 6.4 %collective-permute-start.18 = (f32[64,256]{1,0:T(8,128)S(1)}, f32[64,256]{1,0:T(8,128)S(1)}, u32[]{:S(2)}, u32[]{:S(2)}) collective-permute-start(f32[64,256]{1,0:T(8,128)S(1)} %get-tuple-element.61.refs_2_), channel_id=1, source_target_pairs={{0,1},{1,0},{2,3},{3,2},{4,5},{5,4},{6,7},{7,6},{8,9},{9,8},{10,11... | collective-permute-start | bytes 196616 | tf_op jit(solution)/shard_map/ppermute | solution.py:33
  46.4 10.7 %collective-permute-start.21 = (f32[64,256]{1,0:T(8,128)S(1)}, f32[64,256]{1,0:T(8,128)S(1)}, u32[]{:S(2)}, u32[]{:S(2)}) collective-permute-start(f32[64,256]{1,0:T(8,128)S(1)} %get-tuple-element.65.refs_3_), channel_id=1, source_target_pairs={{0,2},{1,3},{2,0},{3,1},{4,6},{5,7},{6,4},{7,5},{8,10},{9,11},{10,... | collective-permute-start | bytes 196616 | tf_op jit(solution)/shard_map/ppermute | solution.py:33
  49.7 7.6 %collective-permute-start.25 = (f32[64,256]{1,0:T(8,128)S(1)}, f32[64,256]{1,0:T(8,128)S(1)}, u32[]{:S(2)}, u32[]{:S(2)}) collective-permute-start(f32[64,256]{1,0:T(8,128)S(1)} %get-tuple-element.65.refs_3_), channel_id=1, source_target_pairs={{0,3},{1,2},{2,1},{3,0},{4,7},{5,6},{6,5},{7,4},{8,11},{9,10},{10,... | collective-permute-start | bytes 196616 | tf_op jit(solution)/shard_map/ppermute | solution.py:33
  50.2 7.0 %collective-permute-start.24 = (f32[64,256]{1,0:T(8,128)S(1)}, f32[64,256]{1,0:T(8,128)S(1)}, u32[]{:S(2)}, u32[]{:S(2)}) collective-permute-start(f32[64,256]{1,0:T(8,128)S(1)} %get-tuple-element.65.refs_3_), channel_id=1, source_target_pairs={{0,1},{1,0},{2,3},{3,2},{4,5},{5,4},{6,7},{7,6},{8,9},{9,8},{10,11... | collective-permute-start | bytes 196616 | tf_op jit(solution)/shard_map/ppermute | solution.py:33
  51.7 10.6 %collective-permute-start.23 = (f32[64,256]{1,0:T(8,128)S(1)}, f32[64,256]{1,0:T(8,128)S(1)}, u32[]{:S(2)}, u32[]{:S(2)}) collective-permute-start(f32[64,256]{1,0:T(8,128)S(1)} %get-tuple-element.64), channel_id=1, source_target_pairs={{0,2},{1,3},{2,0},{3,1},{4,6},{5,7},{6,4},{7,5},{8,10},{9,11},{10,... | collective-permute-start | bytes 196616 | tf_op jit(solution)/shard_map/ppermute | solution.py:33
  56.6 6.3 %collective-permute-start.26 = (f32[64,256]{1,0:T(8,128)S(1)}, f32[64,256]{1,0:T(8,128)S(1)}, u32[]{:S(2)}, u32[]{:S(2)}) collective-permute-start(f32[64,256]{1,0:T(8,128)S(1)} %get-tuple-element.64), channel_id=1, source_target_pairs={{0,3},{1,2},{2,1},{3,0},{4,7},{5,6},{6,5},{7,4},{8,11},{9,10},{10,... | collective-permute-start | bytes 196616 | tf_op jit(solution)/shard_map/ppermute | solution.py:33
  57.1 5.3 %collective-permute-start.22 = (f32[64,256]{1,0:T(8,128)S(1)}, f32[64,256]{1,0:T(8,128)S(1)}, u32[]{:S(2)}, u32[]{:S(2)}) collective-permute-start(f32[64,256]{1,0:T(8,128)S(1)} %get-tuple-element.64), channel_id=1, source_target_pairs={{0,1},{1,0},{2,3},{3,2},{4,5},{5,4},{6,7},{7,6},{8,9},{9,8},{10,11... | collective-permute-start | bytes 196616 | tf_op jit(solution)/shard_map/ppermute | solution.py:33
  57.9 9.9 %collective-permute-start.28 = (f32[64,256]{1,0:T(8,128)S(1)}, f32[64,256]{1,0:T(8,128)S(1)}, u32[]{:S(2)}, u32[]{:S(2)}) collective-permute-start(f32[64,256]{1,0:T(8,128)S(1)} %get-tuple-element.67), channel_id=1, source_target_pairs={{0,2},{1,3},{2,0},{3,1},{4,6},{5,7},{6,4},{7,5},{8,10},{9,11},{10,... | collective-permute-start | bytes 196616 | tf_op jit(solution)/shard_map/ppermute | solution.py:33
  61.8 6.2 %collective-permute-start.29 = (f32[64,256]{1,0:T(8,128)S(1)}, f32[64,256]{1,0:T(8,128)S(1)}, u32[]{:S(2)}, u32[]{:S(2)}) collective-permute-start(f32[64,256]{1,0:T(8,128)S(1)} %get-tuple-element.67), channel_id=1, source_target_pairs={{0,3},{1,2},{2,1},{3,0},{4,7},{5,6},{6,5},{7,4},{8,11},{9,10},{10,... | collective-permute-start | bytes 196616 | tf_op jit(solution)/shard_map/ppermute | solution.py:33
  62.3 5.7 %collective-permute-start.27 = (f32[64,256]{1,0:T(8,128)S(1)}, f32[64,256]{1,0:T(8,128)S(1)}, u32[]{:S(2)}, u32[]{:S(2)}) collective-permute-start(f32[64,256]{1,0:T(8,128)S(1)} %get-tuple-element.67), channel_id=1, source_target_pairs={{0,1},{1,0},{2,3},{3,2},{4,5},{5,4},{6,7},{7,6},{8,9},{9,8},{10,11... | collective-permute-start | bytes 196616 | tf_op jit(solution)/shard_map/ppermute | solution.py:33
  63.5 10.4 %collective-permute-start.31 = (f32[64,256]{1,0:T(8,128)S(1)}, f32[64,256]{1,0:T(8,128)S(1)}, u32[]{:S(2)}, u32[]{:S(2)}) collective-permute-start(f32[64,256]{1,0:T(8,128)S(1)} %get-tuple-element.69.refs_4_), channel_id=1, source_target_pairs={{0,2},{1,3},{2,0},{3,1},{4,6},{5,7},{6,4},{7,5},{8,10},{9,11},{10,... | collective-permute-start | bytes 196616 | tf_op jit(solution)/shard_map/ppermute | solution.py:33
  66.9 7.1 %collective-permute-start.32 = (f32[64,256]{1,0:T(8,128)S(1)}, f32[64,256]{1,0:T(8,128)S(1)}, u32[]{:S(2)}, u32[]{:S(2)}) collective-permute-start(f32[64,256]{1,0:T(8,128)S(1)} %get-tuple-element.69.refs_4_), channel_id=1, source_target_pairs={{0,3},{1,2},{2,1},{3,0},{4,7},{5,6},{6,5},{7,4},{8,11},{9,10},{10,... | collective-permute-start | bytes 196616 | tf_op jit(solution)/shard_map/ppermute | solution.py:33
  67.9 6.1 %collective-permute-start.30 = (f32[64,256]{1,0:T(8,128)S(1)}, f32[64,256]{1,0:T(8,128)S(1)}, u32[]{:S(2)}, u32[]{:S(2)}) collective-permute-start(f32[64,256]{1,0:T(8,128)S(1)} %get-tuple-element.69.refs_4_), channel_id=1, source_target_pairs={{0,1},{1,0},{2,3},{3,2},{4,5},{5,4},{6,7},{7,6},{8,9},{9,8},{10,11... | collective-permute-start | bytes 196616 | tf_op jit(solution)/shard_map/ppermute | solution.py:33
  68.7 10.4 %collective-permute-start.33 = (f32[64,256]{1,0:T(8,128)S(1)}, f32[64,256]{1,0:T(8,128)S(1)}, u32[]{:S(2)}, u32[]{:S(2)}) collective-permute-start(f32[64,256]{1,0:T(8,128)S(1)} %get-tuple-element.73.refs_5_), channel_id=1, source_target_pairs={{0,2},{1,3},{2,0},{3,1},{4,6},{5,7},{6,4},{7,5},{8,10},{9,11},{10,... | collective-permute-start | bytes 196616 | tf_op jit(solution)/shard_map/ppermute | solution.py:33
  72.1 7.7 %collective-permute-start.37 = (f32[64,256]{1,0:T(8,128)S(1)}, f32[64,256]{1,0:T(8,128)S(1)}, u32[]{:S(2)}, u32[]{:S(2)}) collective-permute-start(f32[64,256]{1,0:T(8,128)S(1)} %get-tuple-element.73.refs_5_), channel_id=1, source_target_pairs={{0,3},{1,2},{2,1},{3,0},{4,7},{5,6},{6,5},{7,4},{8,11},{9,10},{10,... | collective-permute-start | bytes 196616 | tf_op jit(solution)/shard_map/ppermute | solution.py:33
  73.9 5.9 %collective-permute-start.36 = (f32[64,256]{1,0:T(8,128)S(1)}, f32[64,256]{1,0:T(8,128)S(1)}, u32[]{:S(2)}, u32[]{:S(2)}) collective-permute-start(f32[64,256]{1,0:T(8,128)S(1)} %get-tuple-element.73.refs_5_), channel_id=1, source_target_pairs={{0,1},{1,0},{2,3},{3,2},{4,5},{5,4},{6,7},{7,6},{8,9},{9,8},{10,11... | collective-permute-start | bytes 196616 | tf_op jit(solution)/shard_map/ppermute | solution.py:33
  74.7 10.5 %collective-permute-start.35 = (f32[64,256]{1,0:T(8,128)S(1)}, f32[64,256]{1,0:T(8,128)S(1)}, u32[]{:S(2)}, u32[]{:S(2)}) collective-permute-start(f32[64,256]{1,0:T(8,128)S(1)} %get-tuple-element.72), channel_id=1, source_target_pairs={{0,2},{1,3},{2,0},{3,1},{4,6},{5,7},{6,4},{7,5},{8,10},{9,11},{10,... | collective-permute-start | bytes 196616 | tf_op jit(solution)/shard_map/ppermute | solution.py:33
  78.3 6.9 %collective-permute-start.38 = (f32[64,256]{1,0:T(8,128)S(1)}, f32[64,256]{1,0:T(8,128)S(1)}, u32[]{:S(2)}, u32[]{:S(2)}) collective-permute-start(f32[64,256]{1,0:T(8,128)S(1)} %get-tuple-element.72), channel_id=1, source_target_pairs={{0,3},{1,2},{2,1},{3,0},{4,7},{5,6},{6,5},{7,4},{8,11},{9,10},{10,... | collective-permute-start | bytes 196616 | tf_op jit(solution)/shard_map/ppermute | solution.py:33
  79.1 6.1 %collective-permute-start.34 = (f32[64,256]{1,0:T(8,128)S(1)}, f32[64,256]{1,0:T(8,128)S(1)}, u32[]{:S(2)}, u32[]{:S(2)}) collective-permute-start(f32[64,256]{1,0:T(8,128)S(1)} %get-tuple-element.72), channel_id=1, source_target_pairs={{0,1},{1,0},{2,3},{3,2},{4,5},{5,4},{6,7},{7,6},{8,9},{9,8},{10,11... | collective-permute-start | bytes 196616 | tf_op jit(solution)/shard_map/ppermute | solution.py:33
  79.9 18.0 %copy-start = (f32[1,1,3,128,1024]{4,3,2,1,0:T(8,128)S(1)}, f32[1,1,3,128,1024]{4,3,2,1,0:T(8,128)}, u32[]{:S(2)}) copy-start(f32[1,1,3,128,1024]{4,3,2,1,0:T(8,128)} %param.13) | copy-start | bytes 4718596
  79.9 18.0 %copy-start.6 = (s32[1,1,3]{2,1,0:T(1,128)S(1)}, s32[1,1,3]{2,1,0:T(1,128)}, u32[]{:S(2)}) copy-start(s32[1,1,3]{2,1,0:T(1,128)} %refs_6_.1) | copy-start | bytes 40
  80.6 9.8 %collective-permute-start.40 = (f32[64,256]{1,0:T(8,128)S(1)}, f32[64,256]{1,0:T(8,128)S(1)}, u32[]{:S(2)}, u32[]{:S(2)}) collective-permute-start(f32[64,256]{1,0:T(8,128)S(1)} %get-tuple-element.75), channel_id=1, source_target_pairs={{0,2},{1,3},{2,0},{3,1},{4,6},{5,7},{6,4},{7,5},{8,10},{9,11},{10,... | collective-permute-start | bytes 196616 | tf_op jit(solution)/shard_map/ppermute | solution.py:33
  83.5 8.5 %collective-permute-start.41 = (f32[64,256]{1,0:T(8,128)S(1)}, f32[64,256]{1,0:T(8,128)S(1)}, u32[]{:S(2)}, u32[]{:S(2)}) collective-permute-start(f32[64,256]{1,0:T(8,128)S(1)} %get-tuple-element.75), channel_id=1, source_target_pairs={{0,3},{1,2},{2,1},{3,0},{4,7},{5,6},{6,5},{7,4},{8,11},{9,10},{10,... | collective-permute-start | bytes 196616 | tf_op jit(solution)/shard_map/ppermute | solution.py:33
  85.2 6.8 %collective-permute-start.39 = (f32[64,256]{1,0:T(8,128)S(1)}, f32[64,256]{1,0:T(8,128)S(1)}, u32[]{:S(2)}, u32[]{:S(2)}) collective-permute-start(f32[64,256]{1,0:T(8,128)S(1)} %get-tuple-element.75), channel_id=1, source_target_pairs={{0,1},{1,0},{2,3},{3,2},{4,5},{5,4},{6,7},{7,6},{8,9},{9,8},{10,11... | collective-permute-start | bytes 196616 | tf_op jit(solution)/shard_map/ppermute | solution.py:33
  85.9 10.4 %collective-permute-start.43 = (f32[64,256]{1,0:T(8,128)S(1)}, f32[64,256]{1,0:T(8,128)S(1)}, u32[]{:S(2)}, u32[]{:S(2)}) collective-permute-start(f32[64,256]{1,0:T(8,128)S(1)} %get-tuple-element.77.refs_6_), channel_id=1, source_target_pairs={{0,2},{1,3},{2,0},{3,1},{4,6},{5,7},{6,4},{7,5},{8,10},{9,11},{10,... | collective-permute-start | bytes 196616 | tf_op jit(solution)/shard_map/ppermute | solution.py:33
  89.6 6.8 %collective-permute-start.44 = (f32[64,256]{1,0:T(8,128)S(1)}, f32[64,256]{1,0:T(8,128)S(1)}, u32[]{:S(2)}, u32[]{:S(2)}) collective-permute-start(f32[64,256]{1,0:T(8,128)S(1)} %get-tuple-element.77.refs_6_), channel_id=1, source_target_pairs={{0,3},{1,2},{2,1},{3,0},{4,7},{5,6},{6,5},{7,4},{8,11},{9,10},{10,... | collective-permute-start | bytes 196616 | tf_op jit(solution)/shard_map/ppermute | solution.py:33
  90.4 6.0 %collective-permute-start.42 = (f32[64,256]{1,0:T(8,128)S(1)}, f32[64,256]{1,0:T(8,128)S(1)}, u32[]{:S(2)}, u32[]{:S(2)}) collective-permute-start(f32[64,256]{1,0:T(8,128)S(1)} %get-tuple-element.77.refs_6_), channel_id=1, source_target_pairs={{0,1},{1,0},{2,3},{3,2},{4,5},{5,4},{6,7},{7,6},{8,9},{9,8},{10,11... | collective-permute-start | bytes 196616 | tf_op jit(solution)/shard_map/ppermute | solution.py:33
  92.7 5.2 %collective-permute-start.46 = (f32[64,256]{1,0:T(8,128)S(1)}, f32[64,256]{1,0:T(8,128)S(1)}, u32[]{:S(2)}, u32[]{:S(2)}) collective-permute-start(f32[64,256]{1,0:T(8,128)S(1)} %get-tuple-element.79.refs_7_), channel_id=1, source_target_pairs={{0,2},{1,3},{2,0},{3,1},{4,6},{5,7},{6,4},{7,5},{8,10},{9,11},{10,... | collective-permute-start | bytes 196616 | tf_op jit(solution)/shard_map/ppermute | solution.py:33
  94.8 6.6 %collective-permute-start.47 = (f32[64,256]{1,0:T(8,128)S(1)}, f32[64,256]{1,0:T(8,128)S(1)}, u32[]{:S(2)}, u32[]{:S(2)}) collective-permute-start(f32[64,256]{1,0:T(8,128)S(1)} %get-tuple-element.79.refs_7_), channel_id=1, source_target_pairs={{0,3},{1,2},{2,1},{3,0},{4,7},{5,6},{6,5},{7,4},{8,11},{9,10},{10,... | collective-permute-start | bytes 196616 | tf_op jit(solution)/shard_map/ppermute | solution.py:33
  96.4 5.0 %collective-permute-start.45 = (f32[64,256]{1,0:T(8,128)S(1)}, f32[64,256]{1,0:T(8,128)S(1)}, u32[]{:S(2)}, u32[]{:S(2)}) collective-permute-start(f32[64,256]{1,0:T(8,128)S(1)} %get-tuple-element.79.refs_7_), channel_id=1, source_target_pairs={{0,1},{1,0},{2,3},{3,2},{4,5},{5,4},{6,7},{7,6},{8,9},{9,8},{10,11... | collective-permute-start | bytes 196616 | tf_op jit(solution)/shard_map/ppermute | solution.py:33
  102.6 1.4 %collective-permute-start.48 = (f32[4,16,512]{2,1,0:T(8,128)S(1)}, f32[4,16,512]{2,1,0:T(8,128)S(1)}, u32[]{:S(2)}, u32[]{:S(2)}) collective-permute-start(f32[4,16,512]{2,1,0:T(8,128)S(1)} %get-tuple-element.83), channel_id=1, source_target_pairs={{0,4},{4,0},{8,12},{12,8},{16,20},{20,16},{24,28},{28,24},{1,5},{5... | collective-permute-start | bytes 393224 | tf_op jit(solution)/shard_map/ppermute | solution.py:281
  104.1 5.3 %collective-permute-start.49 = (f32[2,16,512]{2,1,0:T(8,128)S(1)}, f32[2,16,512]{2,1,0:T(8,128)S(1)}, u32[]{:S(2)}, u32[]{:S(2)}) collective-permute-start(f32[2,16,512]{2,1,0:T(8,128)S(1)} %get-tuple-element.85), channel_id=1, source_target_pairs={{0,24},{4,28},{8,16},{12,20},{16,8},{20,12},{24,0},{28,4},{1,25},{... | collective-permute-start | bytes 196616 | tf_op jit(solution)/shard_map/ppermute | solution.py:81
  106.6 4.3 %collective-permute-start.50 = (f32[2,16,512]{2,1,0:T(8,128)S(1)}, f32[2,16,512]{2,1,0:T(8,128)S(1)}, u32[]{:S(2)}, u32[]{:S(2)}) collective-permute-start(f32[2,16,512]{2,1,0:T(8,128)S(1)} %get-tuple-element.86), channel_id=1, source_target_pairs={{0,16},{4,20},{8,24},{12,28},{16,0},{20,4},{24,8},{28,12},{1,17},{... | collective-permute-start | bytes 196616 | tf_op jit(solution)/shard_map/ppermute | solution.py:81
  107.1 4.3 %collective-permute-start.51 = (f32[2,16,512]{2,1,0:T(8,128)S(1)}, f32[2,16,512]{2,1,0:T(8,128)S(1)}, u32[]{:S(2)}, u32[]{:S(2)}) collective-permute-start(f32[2,16,512]{2,1,0:T(8,128)S(1)} %get-tuple-element.87), channel_id=1, source_target_pairs={{0,8},{4,12},{8,0},{12,4},{16,24},{20,28},{24,16},{28,20},{1,9},{5... | collective-permute-start | bytes 196616 | tf_op jit(solution)/shard_map/ppermute | solution.py:81
  111.7 5.7 %collective-permute-start.52 = (f32[16,1024]{1,0:T(8,128)S(1)}, f32[16,1024]{1,0:T(8,128)S(1)}, u32[]{:S(2)}, u32[]{:S(2)}) collective-permute-start(f32[16,1024]{1,0:T(8,128)S(1)} %get-tuple-element.89.refs_2_.refs_0_), channel_id=1, source_target_pairs={{0,2},{1,3},{2,0},{3,1},{4,6},{5,7},{6,4},{7,5},{8,10},{9,11},{10,... | collective-permute-start | bytes 196616 | tf_op jit(solution)/shard_map/ppermute | solution.py:33
  112.6 6.2 %collective-permute-start.53 = (f32[16,1024]{1,0:T(8,128)S(1)}, f32[16,1024]{1,0:T(8,128)S(1)}, u32[]{:S(2)}, u32[]{:S(2)}) collective-permute-start(f32[16,1024]{1,0:T(8,128)S(1)} %get-tuple-element.89.refs_2_.refs_0_), channel_id=1, source_target_pairs={{0,3},{1,2},{2,1},{3,0},{4,7},{5,6},{6,5},{7,4},{8,11},{9,10},{10,... | collective-permute-start | bytes 196616 | tf_op jit(solution)/shard_map/ppermute | solution.py:33
  114.2 5.0 %collective-permute-start.54 = (f32[16,1024]{1,0:T(8,128)S(1)}, f32[16,1024]{1,0:T(8,128)S(1)}, u32[]{:S(2)}, u32[]{:S(2)}) collective-permute-start(f32[16,1024]{1,0:T(8,128)S(1)} %get-tuple-element.89.refs_2_.refs_0_), channel_id=1, source_target_pairs={{0,1},{1,0},{2,3},{3,2},{4,5},{5,4},{6,7},{7,6},{8,9},{9,8},{10,11... | collective-permute-start | bytes 196616 | tf_op jit(solution)/shard_map/ppermute | solution.py:33
  119.5 5.1 %collective-permute-start.55 = (f32[16,512]{1,0:T(8,128)S(1)}, f32[16,512]{1,0:T(8,128)S(1)}, u32[]{:S(2)}, u32[]{:S(2)}) collective-permute-start(f32[16,512]{1,0:T(8,128)S(1)} %get-tuple-element.97), channel_id=1, source_target_pairs={{0,2},{1,3},{2,0},{3,1},{4,6},{5,7},{6,4},{7,5},{8,10},{9,11},{10,... | collective-permute-start | bytes 98312 | tf_op jit(solution)/shard_map/ppermute | solution.py:33
  120.6 5.9 %collective-permute-start.56 = (f32[16,512]{1,0:T(8,128)S(1)}, f32[16,512]{1,0:T(8,128)S(1)}, u32[]{:S(2)}, u32[]{:S(2)}) collective-permute-start(f32[16,512]{1,0:T(8,128)S(1)} %get-tuple-element.98), channel_id=1, source_target_pairs={{0,3},{1,2},{2,1},{3,0},{4,7},{5,6},{6,5},{7,4},{8,11},{9,10},{10,... | collective-permute-start | bytes 98312 | tf_op jit(solution)/shard_map/ppermute | solution.py:33
  122.3 4.3 %collective-permute-start.57 = (f32[16,512]{1,0:T(8,128)S(1)}, f32[16,512]{1,0:T(8,128)S(1)}, u32[]{:S(2)}, u32[]{:S(2)}) collective-permute-start(f32[16,512]{1,0:T(8,128)S(1)} %get-tuple-element.99), channel_id=1, source_target_pairs={{0,1},{1,0},{2,3},{3,2},{4,5},{5,4},{6,7},{7,6},{8,9},{9,8},{10,11... | collective-permute-start | bytes 98312 | tf_op jit(solution)/shard_map/ppermute | solution.py:33
  127.0 4.7 %collective-permute-start.58 = (f32[16,256]{1,0:T(8,128)S(1)}, f32[16,256]{1,0:T(8,128)S(1)}, u32[]{:S(2)}, u32[]{:S(2)}) collective-permute-start(f32[16,256]{1,0:T(8,128)S(1)} %shard_map.124.refs_0_), channel_id=1, source_target_pairs={{0,2},{1,3},{2,0},{3,1},{4,6},{5,7},{6,4},{7,5},{8,10},{9,11},{10,... | collective-permute-start | bytes 49160 | tf_op jit(solution)/shard_map/ppermute | solution.py:33
  127.9 5.5 %collective-permute-start.59 = (f32[16,256]{1,0:T(8,128)S(1)}, f32[16,256]{1,0:T(8,128)S(1)}, u32[]{:S(2)}, u32[]{:S(2)}) collective-permute-start(f32[16,256]{1,0:T(8,128)S(1)} %shard_map.124.refs_0_), channel_id=1, source_target_pairs={{0,3},{1,2},{2,1},{3,0},{4,7},{5,6},{6,5},{7,4},{8,11},{9,10},{10,... | collective-permute-start | bytes 49160 | tf_op jit(solution)/shard_map/ppermute | solution.py:33
  129.8 3.8 %collective-permute-start.60 = (f32[16,256]{1,0:T(8,128)S(1)}, f32[16,256]{1,0:T(8,128)S(1)}, u32[]{:S(2)}, u32[]{:S(2)}) collective-permute-start(f32[16,256]{1,0:T(8,128)S(1)} %shard_map.124.refs_0_), channel_id=1, source_target_pairs={{0,1},{1,0},{2,3},{3,2},{4,5},{5,4},{6,7},{7,6},{8,9},{9,8},{10,11... | collective-permute-start | bytes 49160 | tf_op jit(solution)/shard_map/ppermute | solution.py:33
  (7 other events, 93.6 us)

commit v26 on v22

--- a/solution.py
+++ b/solution.py
@@ -494,7 +494,8 @@
         for i in range(streams):
             turn_taken = step > 0 and last is not None
             ties = [(1, last[0][2][1])] if step * streams + i > streams else []
-            pieces = gather_rows(values[i], ties)
+            early = step == 1 and i == 0
+            pieces = gather_rows(values[i], ties, early)
             if step == 1 and i == 0:
                 later = turn(rhs_local, 1, supernodes, streams, pieces[1][1])
             if turn_taken:

time: 134 us -> 134 us (level)
  waiting for transfers between devices: 22.9 us -> 24.7 us
  starting transfers between devices: 90.2 us -> 88.5 us
    ppermute x57, waiting for transfers between devices: 18.9 us -> 20.6 us  [send(): return lax.ppermute(value, axis, pairs)]
    ppermute x57, starting transfers between devices: 86.6 us -> 84.9 us  [send(): return lax.ppermute(value, axis, pairs)]
  transfers between devices with their start and end apart: 61 -> 61, of which waited for: 18 -> 27; matrix products, arithmetic and copies ran while one was open for 7% -> 7% of each run, Pallas kernels for 3% -> 3%
where the time goes in v26:
time: 134 us; the launch traced here: 133 us
  starting transfers between devices  88.5 us (66%)
  waiting for transfers between devices  24.7 us (18%)
  matrix products  7.54 us (6%)
  Pallas kernels  7.53 us (6%)
  between operations  2.01 us (1%)
  local copies, waits for them, and re-layouts  1.82 us (1%)
  other arithmetic  1.41 us (1%)
    ppermute x57, starting transfers between devices, send(): return lax.ppermute(value, axis, pairs)  84.9 us
    ppermute x57, waiting for transfers between devices, send(): return lax.ppermute(value, axis, pairs)  20.6 us
    dot_general x12, matrix products, contract_last(): lax.dot_general(left, right, (((left.ndim - 1,), (right.ndim - 1,)), ((),...  7.54 us
    pallas_call x13, Pallas kernels, local_kernel(): pl.pallas_call(body, out_shape=list(outs), in_specs=specs or [VMEM] * len...  7.53 us
    ppermute x3, starting transfers between devices, swap(): return lax.ppermute(value, axis, pairs)  3.55 us
    ppermute x3, waiting for transfers between devices, swap(): return lax.ppermute(value, axis, pairs)  2.73 us
  transfers between devices with their start and end apart: 61, of which 27 were waited for; matrix products, arithmetic and copies ran while one was open for 7% of the time, Pallas kernels for 3%

profile of v26, /device:TPU:0, one launch (start us, length us, event | category | flops | bytes accessed | tf_op | source)
XLA Modules:
  0.0 133.5 jit_solution(8990329390591015489)
XLA Ops:
  0.6 1.0 copy-done.2
  1.9 3.1 %collective-permute-start = (f32[64,256]{1,0:T(8,128)S(1)}, f32[64,256]{1,0:T(8,128)S(1)}, u32[]{:S(2)}, u32[]{:S(2)}) collective-permute-start(f32[64,256]{1,0:T(8,128)S(1)} %get-tuple-element.52.refs_0_), channel_id=1, source_target_pairs={{0,1},{1,0},{2,3},{3,2},{4,5},{5,4},{6,7},{7,6},{8,9},{9,8},{10,11... | collective-permute-start | bytes 196616 | tf_op jit(solution)/shard_map/ppermute | solution.py:33
  5.0 2.6 %collective-permute-start.1 = (f32[64,256]{1,0:T(8,128)S(1)}, f32[64,256]{1,0:T(8,128)S(1)}, u32[]{:S(2)}, u32[]{:S(2)}) collective-permute-start(f32[64,256]{1,0:T(8,128)S(1)} %get-tuple-element.52.refs_0_), channel_id=1, source_target_pairs={{0,2},{1,3},{2,0},{3,1},{4,6},{5,7},{6,4},{7,5},{8,10},{9,11},{10,... | collective-permute-start | bytes 196616 | tf_op jit(solution)/shard_map/ppermute | solution.py:33
  7.6 0.9 collective-permute-start.3
  8.5 3.5 %collective-permute-start.4 = (f32[64,256]{1,0:T(8,128)S(1)}, f32[64,256]{1,0:T(8,128)S(1)}, u32[]{:S(2)}, u32[]{:S(2)}) collective-permute-start(f32[64,256]{1,0:T(8,128)S(1)} %get-tuple-element.53.refs_0_), channel_id=1, source_target_pairs={{0,2},{1,3},{2,0},{3,1},{4,6},{5,7},{6,4},{7,5},{8,10},{9,11},{10,... | collective-permute-start | bytes 196616 | tf_op jit(solution)/shard_map/ppermute | solution.py:33
  12.0 1.4 %fusion = (bf16[1,256,1024]{2,1,0:T(8,128)(2,1)S(1)}, bf16[1,256,1024]{2,1,0:T(8,128)(2,1)S(1)}) fusion(f32[1,4,256,1024]{3,2,1,0:T(8,128)} %param.11), kind=kLoop, calls=%fused_computation.2 | loop fusion | flops 1048576 | bytes 2097152 | tf_op jit(solution)/shard_map/convert_element_type | solution.py:487
  14.6 5.8 %collective-permute-start.6 = (f32[64,256]{1,0:T(8,128)S(1)}, f32[64,256]{1,0:T(8,128)S(1)}, u32[]{:S(2)}, u32[]{:S(2)}) collective-permute-start(f32[64,256]{1,0:T(8,128)S(1)} %shard_map.114.refs_0_), channel_id=1, source_target_pairs={{0,2},{1,3},{2,0},{3,1},{4,6},{5,7},{6,4},{7,5},{8,10},{9,11},{10,... | collective-permute-start | bytes 196616 | tf_op jit(solution)/shard_map/ppermute | solution.py:33
  21.6 3.8 %collective-permute-start.9 = (f32[64,256]{1,0:T(8,128)S(1)}, f32[64,256]{1,0:T(8,128)S(1)}, u32[]{:S(2)}, u32[]{:S(2)}) collective-permute-start(f32[64,256]{1,0:T(8,128)S(1)} %shard_map.115.refs_1_), channel_id=1, source_target_pairs={{0,2},{1,3},{2,0},{3,1},{4,6},{5,7},{6,4},{7,5},{8,10},{9,11},{10,... | collective-permute-start | bytes 196616 | tf_op jit(solution)/shard_map/ppermute | solution.py:33
  25.9 1.4 %collective-permute-done.7 = f32[64,256]{1,0:T(8,128)S(1)} collective-permute-done((f32[64,256]{1,0:T(8,128)S(1)}, f32[64,256]{1,0:T(8,128)S(1)}, u32[]{:S(2)}, u32[]{:S(2)}) %collective-permute-start.7) | collective-permute-done | bytes 65568 | tf_op jit(solution)/shard_map/ppermute | solution.py:33
  27.3 0.8 collective-permute-start.12
  29.2 1.9 %collective-permute-start.11 = (f32[64,256]{1,0:T(8,128)S(1)}, f32[64,256]{1,0:T(8,128)S(1)}, u32[]{:S(2)}, u32[]{:S(2)}) collective-permute-start(f32[64,256]{1,0:T(8,128)S(1)} %get-tuple-element.56), channel_id=1, source_target_pairs={{0,2},{1,3},{2,0},{3,1},{4,6},{5,7},{6,4},{7,5},{8,10},{9,11},{10,... | collective-permute-start | bytes 196616 | tf_op jit(solution)/shard_map/ppermute | solution.py:33
  31.1 1.7 %collective-permute-start.14 = (f32[64,256]{1,0:T(8,128)S(1)}, f32[64,256]{1,0:T(8,128)S(1)}, u32[]{:S(2)}, u32[]{:S(2)}) collective-permute-start(f32[64,256]{1,0:T(8,128)S(1)} %get-tuple-element.56), channel_id=1, source_target_pairs={{0,3},{1,2},{2,1},{3,0},{4,7},{5,6},{6,5},{7,4},{8,11},{9,10},{10,... | collective-permute-start | bytes 196616 | tf_op jit(solution)/shard_map/ppermute | solution.py:33
  33.4 0.6 constant_dynamic-update-slice_fusion.43
  34.1 2.2 %collective-permute-start.16 = (f32[64,256]{1,0:T(8,128)S(1)}, f32[64,256]{1,0:T(8,128)S(1)}, u32[]{:S(2)}, u32[]{:S(2)}) collective-permute-start(f32[64,256]{1,0:T(8,128)S(1)} %get-tuple-element.59), channel_id=1, source_target_pairs={{0,2},{1,3},{2,0},{3,1},{4,6},{5,7},{6,4},{7,5},{8,10},{9,11},{10,... | collective-permute-start | bytes 196616 | tf_op jit(solution)/shard_map/ppermute | solution.py:33
  36.3 1.7 %collective-permute-start.17 = (f32[64,256]{1,0:T(8,128)S(1)}, f32[64,256]{1,0:T(8,128)S(1)}, u32[]{:S(2)}, u32[]{:S(2)}) collective-permute-start(f32[64,256]{1,0:T(8,128)S(1)} %get-tuple-element.59), channel_id=1, source_target_pairs={{0,3},{1,2},{2,1},{3,0},{4,7},{5,6},{6,5},{7,4},{8,11},{9,10},{10,... | collective-permute-start | bytes 196616 | tf_op jit(solution)/shard_map/ppermute | solution.py:33
  38.0 0.7 collective-permute-done.10
  39.4 2.0 %collective-permute-start.19 = (f32[64,256]{1,0:T(8,128)S(1)}, f32[64,256]{1,0:T(8,128)S(1)}, u32[]{:S(2)}, u32[]{:S(2)}) collective-permute-start(f32[64,256]{1,0:T(8,128)S(1)} %get-tuple-element.61.refs_2_), channel_id=1, source_target_pairs={{0,2},{1,3},{2,0},{3,1},{4,6},{5,7},{6,4},{7,5},{8,10},{9,11},{10,... | collective-permute-start | bytes 196616 | tf_op jit(solution)/shard_map/ppermute | solution.py:33
  41.5 2.7 %collective-permute-start.20 = (f32[64,256]{1,0:T(8,128)S(1)}, f32[64,256]{1,0:T(8,128)S(1)}, u32[]{:S(2)}, u32[]{:S(2)}) collective-permute-start(f32[64,256]{1,0:T(8,128)S(1)} %get-tuple-element.61.refs_2_), channel_id=1, source_target_pairs={{0,3},{1,2},{2,1},{3,0},{4,7},{5,6},{6,5},{7,4},{8,11},{9,10},{10,... | collective-permute-start | bytes 196616 | tf_op jit(solution)/shard_map/ppermute | solution.py:33
  45.1 3.8 %collective-permute-start.21 = (f32[64,256]{1,0:T(8,128)S(1)}, f32[64,256]{1,0:T(8,128)S(1)}, u32[]{:S(2)}, u32[]{:S(2)}) collective-permute-start(f32[64,256]{1,0:T(8,128)S(1)} %get-tuple-element.65.refs_3_), channel_id=1, source_target_pairs={{0,2},{1,3},{2,0},{3,1},{4,6},{5,7},{6,4},{7,5},{8,10},{9,11},{10,... | collective-permute-start | bytes 196616 | tf_op jit(solution)/shard_map/ppermute | solution.py:33
  50.3 3.7 %collective-permute-start.23 = (f32[64,256]{1,0:T(8,128)S(1)}, f32[64,256]{1,0:T(8,128)S(1)}, u32[]{:S(2)}, u32[]{:S(2)}) collective-permute-start(f32[64,256]{1,0:T(8,128)S(1)} %get-tuple-element.64), channel_id=1, source_target_pairs={{0,2},{1,3},{2,0},{3,1},{4,6},{5,7},{6,4},{7,5},{8,10},{9,11},{10,... | collective-permute-start | bytes 196616 | tf_op jit(solution)/shard_map/ppermute | solution.py:33
  54.7 1.2 collective-permute-done.24
  55.9 0.6 constant_dynamic-update-slice_fusion.27
  56.6 2.9 %collective-permute-start.28 = (f32[64,256]{1,0:T(8,128)S(1)}, f32[64,256]{1,0:T(8,128)S(1)}, u32[]{:S(2)}, u32[]{:S(2)}) collective-permute-start(f32[64,256]{1,0:T(8,128)S(1)} %get-tuple-element.67), channel_id=1, source_target_pairs={{0,2},{1,3},{2,0},{3,1},{4,6},{5,7},{6,4},{7,5},{8,10},{9,11},{10,... | collective-permute-start | bytes 196616 | tf_op jit(solution)/shard_map/ppermute | solution.py:33
  59.5 0.9 collective-permute-start.29
  60.9 0.6 constant_dynamic-update-slice_fusion.23
  61.5 3.1 %collective-permute-start.31 = (f32[64,256]{1,0:T(8,128)S(1)}, f32[64,256]{1,0:T(8,128)S(1)}, u32[]{:S(2)}, u32[]{:S(2)}) collective-permute-start(f32[64,256]{1,0:T(8,128)S(1)} %get-tuple-element.69.refs_4_), channel_id=1, source_target_pairs={{0,2},{1,3},{2,0},{3,1},{4,6},{5,7},{6,4},{7,5},{8,10},{9,11},{10,... | collective-permute-start | bytes 196616 | tf_op jit(solution)/shard_map/ppermute | solution.py:33
  64.6 2.1 %collective-permute-start.32 = (f32[64,256]{1,0:T(8,128)S(1)}, f32[64,256]{1,0:T(8,128)S(1)}, u32[]{:S(2)}, u32[]{:S(2)}) collective-permute-start(f32[64,256]{1,0:T(8,128)S(1)} %get-tuple-element.69.refs_4_), channel_id=1, source_target_pairs={{0,3},{1,2},{2,1},{3,0},{4,7},{5,6},{6,5},{7,4},{8,11},{9,10},{10,... | collective-permute-start | bytes 196616 | tf_op jit(solution)/shard_map/ppermute | solution.py:33
  67.8 3.6 %collective-permute-start.33 = (f32[64,256]{1,0:T(8,128)S(1)}, f32[64,256]{1,0:T(8,128)S(1)}, u32[]{:S(2)}, u32[]{:S(2)}) collective-permute-start(f32[64,256]{1,0:T(8,128)S(1)} %get-tuple-element.73.refs_5_), channel_id=1, source_target_pairs={{0,2},{1,3},{2,0},{3,1},{4,6},{5,7},{6,4},{7,5},{8,10},{9,11},{10,... | collective-permute-start | bytes 196616 | tf_op jit(solution)/shard_map/ppermute | solution.py:33
  73.1 3.4 %collective-permute-start.35 = (f32[64,256]{1,0:T(8,128)S(1)}, f32[64,256]{1,0:T(8,128)S(1)}, u32[]{:S(2)}, u32[]{:S(2)}) collective-permute-start(f32[64,256]{1,0:T(8,128)S(1)} %get-tuple-element.72), channel_id=1, source_target_pairs={{0,2},{1,3},{2,0},{3,1},{4,6},{5,7},{6,4},{7,5},{8,10},{9,11},{10,... | collective-permute-start | bytes 196616 | tf_op jit(solution)/shard_map/ppermute | solution.py:33
  76.5 1.5 %collective-permute-start.38 = (f32[64,256]{1,0:T(8,128)S(1)}, f32[64,256]{1,0:T(8,128)S(1)}, u32[]{:S(2)}, u32[]{:S(2)}) collective-permute-start(f32[64,256]{1,0:T(8,128)S(1)} %get-tuple-element.72), channel_id=1, source_target_pairs={{0,3},{1,2},{2,1},{3,0},{4,7},{5,6},{6,5},{7,4},{8,11},{9,10},{10,... | collective-permute-start | bytes 196616 | tf_op jit(solution)/shard_map/ppermute | solution.py:33
  78.5 0.6 constant_dynamic-update-slice_fusion.11
  79.1 2.9 %collective-permute-start.40 = (f32[64,256]{1,0:T(8,128)S(1)}, f32[64,256]{1,0:T(8,128)S(1)}, u32[]{:S(2)}, u32[]{:S(2)}) collective-permute-start(f32[64,256]{1,0:T(8,128)S(1)} %get-tuple-element.75), channel_id=1, source_target_pairs={{0,2},{1,3},{2,0},{3,1},{4,6},{5,7},{6,4},{7,5},{8,10},{9,11},{10,... | collective-permute-start | bytes 196616 | tf_op jit(solution)/shard_map/ppermute | solution.py:33
  82.0 1.2 collective-permute-start.41
  84.2 3.0 %collective-permute-start.43 = (f32[64,256]{1,0:T(8,128)S(1)}, f32[64,256]{1,0:T(8,128)S(1)}, u32[]{:S(2)}, u32[]{:S(2)}) collective-permute-start(f32[64,256]{1,0:T(8,128)S(1)} %get-tuple-element.77.refs_6_), channel_id=1, source_target_pairs={{0,2},{1,3},{2,0},{3,1},{4,6},{5,7},{6,4},{7,5},{8,10},{9,11},{10,... | collective-permute-start | bytes 196616 | tf_op jit(solution)/shard_map/ppermute | solution.py:33
  87.2 2.1 %collective-permute-start.44 = (f32[64,256]{1,0:T(8,128)S(1)}, f32[64,256]{1,0:T(8,128)S(1)}, u32[]{:S(2)}, u32[]{:S(2)}) collective-permute-start(f32[64,256]{1,0:T(8,128)S(1)} %get-tuple-element.77.refs_6_), channel_id=1, source_target_pairs={{0,3},{1,2},{2,1},{3,0},{4,7},{5,6},{6,5},{7,4},{8,11},{9,10},{10,... | collective-permute-start | bytes 196616 | tf_op jit(solution)/shard_map/ppermute | solution.py:33
  89.7 0.6 constant_dynamic-update-slice_fusion.3
  90.3 3.6 %collective-permute-start.46 = (f32[64,256]{1,0:T(8,128)S(1)}, f32[64,256]{1,0:T(8,128)S(1)}, u32[]{:S(2)}, u32[]{:S(2)}) collective-permute-start(f32[64,256]{1,0:T(8,128)S(1)} %get-tuple-element.79.refs_7_), channel_id=1, source_target_pairs={{0,2},{1,3},{2,0},{3,1},{4,6},{5,7},{6,4},{7,5},{8,10},{9,11},{10,... | collective-permute-start | bytes 196616 | tf_op jit(solution)/shard_map/ppermute | solution.py:33
  93.9 0.6 collective-permute-start.47
  94.8 1.4 %collective-permute-done.46 = f32[64,256]{1,0:T(8,128)S(1)} collective-permute-done((f32[64,256]{1,0:T(8,128)S(1)}, f32[64,256]{1,0:T(8,128)S(1)}, u32[]{:S(2)}, u32[]{:S(2)}) %collective-permute-start.46) | collective-permute-done | bytes 65568 | tf_op jit(solution)/shard_map/ppermute | solution.py:33
  96.2 1.2 shard_map.117.refs_0_
  97.4 1.4 %collective-permute-done.45 = f32[64,256]{1,0:T(8,128)S(1)} collective-permute-done((f32[64,256]{1,0:T(8,128)S(1)}, f32[64,256]{1,0:T(8,128)S(1)}, u32[]{:S(2)}, u32[]{:S(2)}) %collective-permute-start.45) | collective-permute-done | bytes 65568 | tf_op jit(solution)/shard_map/ppermute | solution.py:33
  98.8 1.1 collective-permute-done.47
  99.9 1.2 shard_map.118
  101.2 1.3 collective-permute-done.48.refs_1_
  102.6 2.5 %collective-permute-start.49 = (f32[2,16,512]{2,1,0:T(8,128)S(1)}, f32[2,16,512]{2,1,0:T(8,128)S(1)}, u32[]{:S(2)}, u32[]{:S(2)}) collective-permute-start(f32[2,16,512]{2,1,0:T(8,128)S(1)} %get-tuple-element.85), channel_id=1, source_target_pairs={{0,24},{4,28},{8,16},{12,20},{16,8},{20,12},{24,0},{28,4},{1,25},{... | collective-permute-start | bytes 196616 | tf_op jit(solution)/shard_map/ppermute | solution.py:81
  106.2 1.0 shard_map.119
  107.2 0.7 collective-permute-done.49.refs_1_
  107.9 1.5 %collective-permute-done.50.refs_2_ = f32[2,16,512]{2,1,0:T(8,128)S(1)} collective-permute-done((f32[2,16,512]{2,1,0:T(8,128)S(1)}, f32[2,16,512]{2,1,0:T(8,128)S(1)}, u32[]{:S(2)}, u32[]{:S(2)}) %collective-permute-start.50) | collective-permute-done | bytes 65568 | tf_op jit(solution)/shard_map/ppermute | solution.py:81
  110.3 1.4 %collective-permute-start.52 = (f32[16,1024]{1,0:T(8,128)S(1)}, f32[16,1024]{1,0:T(8,128)S(1)}, u32[]{:S(2)}, u32[]{:S(2)}) collective-permute-start(f32[16,1024]{1,0:T(8,128)S(1)} %get-tuple-element.89.refs_2_.refs_0_), channel_id=1, source_target_pairs={{0,2},{1,3},{2,0},{3,1},{4,6},{5,7},{6,4},{7,5},{8,10},{9,11},{10,... | collective-permute-start | bytes 196616 | tf_op jit(solution)/shard_map/ppermute | solution.py:33
  111.7 0.8 collective-permute-start.53
  112.5 1.3 collective-permute-start.54
  114.3 1.8 %collective-permute-done.52.refs_1_ = f32[16,1024]{1,0:T(8,128)S(1)} collective-permute-done((f32[16,1024]{1,0:T(8,128)S(1)}, f32[16,1024]{1,0:T(8,128)S(1)}, u32[]{:S(2)}, u32[]{:S(2)}) %collective-permute-start.52) | collective-permute-done | bytes 65568 | tf_op jit(solution)/shard_map/ppermute | solution.py:33
  116.1 1.6 %collective-permute-done.53.refs_2_ = f32[16,1024]{1,0:T(8,128)S(1)} collective-permute-done((f32[16,1024]{1,0:T(8,128)S(1)}, f32[16,1024]{1,0:T(8,128)S(1)}, u32[]{:S(2)}, u32[]{:S(2)}) %collective-permute-start.53) | collective-permute-done | bytes 65568 | tf_op jit(solution)/shard_map/ppermute | solution.py:33
  118.1 1.4 %collective-permute-start.55 = (f32[16,512]{1,0:T(8,128)S(1)}, f32[16,512]{1,0:T(8,128)S(1)}, u32[]{:S(2)}, u32[]{:S(2)}) collective-permute-start(f32[16,512]{1,0:T(8,128)S(1)} %get-tuple-element.97), channel_id=1, source_target_pairs={{0,2},{1,3},{2,0},{3,1},{4,6},{5,7},{6,4},{7,5},{8,10},{9,11},{10,... | collective-permute-start | bytes 98312 | tf_op jit(solution)/shard_map/ppermute | solution.py:33
  119.5 1.3 %collective-permute-start.56 = (f32[16,512]{1,0:T(8,128)S(1)}, f32[16,512]{1,0:T(8,128)S(1)}, u32[]{:S(2)}, u32[]{:S(2)}) collective-permute-start(f32[16,512]{1,0:T(8,128)S(1)} %get-tuple-element.98), channel_id=1, source_target_pairs={{0,3},{1,2},{2,1},{3,0},{4,7},{5,6},{6,5},{7,4},{8,11},{9,10},{10,... | collective-permute-start | bytes 98312 | tf_op jit(solution)/shard_map/ppermute | solution.py:33
  120.9 0.8 collective-permute-start.57
  121.6 1.7 %collective-permute-done.55.refs_2_ = f32[16,512]{1,0:T(8,128)S(1)} collective-permute-done((f32[16,512]{1,0:T(8,128)S(1)}, f32[16,512]{1,0:T(8,128)S(1)}, u32[]{:S(2)}, u32[]{:S(2)}) %collective-permute-start.55) | collective-permute-done | bytes 32800 | tf_op jit(solution)/shard_map/ppermute | solution.py:33
  123.4 1.9 %collective-permute-done.56.refs_3_ = f32[16,512]{1,0:T(8,128)S(1)} collective-permute-done((f32[16,512]{1,0:T(8,128)S(1)}, f32[16,512]{1,0:T(8,128)S(1)}, u32[]{:S(2)}, u32[]{:S(2)}) %collective-permute-start.56) | collective-permute-done | bytes 32800 | tf_op jit(solution)/shard_map/ppermute | solution.py:33
  125.6 1.3 collective-permute-start.58
  126.9 1.4 %collective-permute-start.59 = (f32[16,256]{1,0:T(8,128)S(1)}, f32[16,256]{1,0:T(8,128)S(1)}, u32[]{:S(2)}, u32[]{:S(2)}) collective-permute-start(f32[16,256]{1,0:T(8,128)S(1)} %shard_map.124.refs_0_), channel_id=1, source_target_pairs={{0,3},{1,2},{2,1},{3,0},{4,7},{5,6},{6,5},{7,4},{8,11},{9,10},{10,... | collective-permute-start | bytes 49160 | tf_op jit(solution)/shard_map/ppermute | solution.py:33
  128.3 0.8 collective-permute-start.60
  129.1 1.1 collective-permute-done.58.refs_1_
  130.3 2.2 %collective-permute-done.59.refs_2_ = f32[16,256]{1,0:T(8,128)S(1)} collective-permute-done((f32[16,256]{1,0:T(8,128)S(1)}, f32[16,256]{1,0:T(8,128)S(1)}, u32[]{:S(2)}, u32[]{:S(2)}) %collective-permute-start.59) | collective-permute-done | bytes 16416 | tf_op jit(solution)/shard_map/ppermute | solution.py:33
  132.5 1.0 shard_map.125
  (162 shorter events, 16.1 us)
Async XLA Ops:
  1.7 26.4 %copy-start.3 = (f32[1,4,256,128]{3,2,1,0:T(8,128)S(1)}, f32[1,4,256,128]{3,2,1,0:T(8,128)}, u32[]{:S(2)}) copy-start(f32[1,4,256,128]{3,2,1,0:T(8,128)} %rhs_ref.3) | copy-start | bytes 1572868
  1.9 10.1 %collective-permute-start = (f32[64,256]{1,0:T(8,128)S(1)}, f32[64,256]{1,0:T(8,128)S(1)}, u32[]{:S(2)}, u32[]{:S(2)}) collective-permute-start(f32[64,256]{1,0:T(8,128)S(1)} %get-tuple-element.52.refs_0_), channel_id=1, source_target_pairs={{0,1},{1,0},{2,3},{3,2},{4,5},{5,4},{6,7},{7,6},{8,9},{9,8},{10,11... | collective-permute-start | bytes 196616 | tf_op jit(solution)/shard_map/ppermute | solution.py:33
  5.0 9.1 %collective-permute-start.1 = (f32[64,256]{1,0:T(8,128)S(1)}, f32[64,256]{1,0:T(8,128)S(1)}, u32[]{:S(2)}, u32[]{:S(2)}) collective-permute-start(f32[64,256]{1,0:T(8,128)S(1)} %get-tuple-element.52.refs_0_), channel_id=1, source_target_pairs={{0,2},{1,3},{2,0},{3,1},{4,6},{5,7},{6,4},{7,5},{8,10},{9,11},{10,... | collective-permute-start | bytes 196616 | tf_op jit(solution)/shard_map/ppermute | solution.py:33
  7.6 6.6 %collective-permute-start.2 = (f32[64,256]{1,0:T(8,128)S(1)}, f32[64,256]{1,0:T(8,128)S(1)}, u32[]{:S(2)}, u32[]{:S(2)}) collective-permute-start(f32[64,256]{1,0:T(8,128)S(1)} %get-tuple-element.52.refs_0_), channel_id=1, source_target_pairs={{0,3},{1,2},{2,1},{3,0},{4,7},{5,6},{6,5},{7,4},{8,11},{9,10},{10,... | collective-permute-start | bytes 196616 | tf_op jit(solution)/shard_map/ppermute | solution.py:33
  7.6 13.3 %collective-permute-start.3 = (f32[64,256]{1,0:T(8,128)S(1)}, f32[64,256]{1,0:T(8,128)S(1)}, u32[]{:S(2)}, u32[]{:S(2)}) collective-permute-start(f32[64,256]{1,0:T(8,128)S(1)} %get-tuple-element.53.refs_0_), channel_id=1, source_target_pairs={{0,1},{1,0},{2,3},{3,2},{4,5},{5,4},{6,7},{7,6},{8,9},{9,8},{10,11... | collective-permute-start | bytes 196616 | tf_op jit(solution)/shard_map/ppermute | solution.py:33
  8.5 12.6 %collective-permute-start.4 = (f32[64,256]{1,0:T(8,128)S(1)}, f32[64,256]{1,0:T(8,128)S(1)}, u32[]{:S(2)}, u32[]{:S(2)}) collective-permute-start(f32[64,256]{1,0:T(8,128)S(1)} %get-tuple-element.53.refs_0_), channel_id=1, source_target_pairs={{0,2},{1,3},{2,0},{3,1},{4,6},{5,7},{6,4},{7,5},{8,10},{9,11},{10,... | collective-permute-start | bytes 196616 | tf_op jit(solution)/shard_map/ppermute | solution.py:33
  12.0 9.1 %collective-permute-start.5 = (f32[64,256]{1,0:T(8,128)S(1)}, f32[64,256]{1,0:T(8,128)S(1)}, u32[]{:S(2)}, u32[]{:S(2)}) collective-permute-start(f32[64,256]{1,0:T(8,128)S(1)} %get-tuple-element.53.refs_0_), channel_id=1, source_target_pairs={{0,3},{1,2},{2,1},{3,0},{4,7},{5,6},{6,5},{7,4},{8,11},{9,10},{10,... | collective-permute-start | bytes 196616 | tf_op jit(solution)/shard_map/ppermute | solution.py:33
  14.6 13.5 %collective-permute-start.6 = (f32[64,256]{1,0:T(8,128)S(1)}, f32[64,256]{1,0:T(8,128)S(1)}, u32[]{:S(2)}, u32[]{:S(2)}) collective-permute-start(f32[64,256]{1,0:T(8,128)S(1)} %shard_map.114.refs_0_), channel_id=1, source_target_pairs={{0,2},{1,3},{2,0},{3,1},{4,6},{5,7},{6,4},{7,5},{8,10},{9,11},{10,... | collective-permute-start | bytes 196616 | tf_op jit(solution)/shard_map/ppermute | solution.py:33
  20.5 6.8 %collective-permute-start.7 = (f32[64,256]{1,0:T(8,128)S(1)}, f32[64,256]{1,0:T(8,128)S(1)}, u32[]{:S(2)}, u32[]{:S(2)}) collective-permute-start(f32[64,256]{1,0:T(8,128)S(1)} %shard_map.114.refs_0_), channel_id=1, source_target_pairs={{0,3},{1,2},{2,1},{3,0},{4,7},{5,6},{6,5},{7,4},{8,11},{9,10},{10,... | collective-permute-start | bytes 196616 | tf_op jit(solution)/shard_map/ppermute | solution.py:33
  20.9 7.6 %collective-permute-start.8 = (f32[64,256]{1,0:T(8,128)S(1)}, f32[64,256]{1,0:T(8,128)S(1)}, u32[]{:S(2)}, u32[]{:S(2)}) collective-permute-start(f32[64,256]{1,0:T(8,128)S(1)} %shard_map.114.refs_0_), channel_id=1, source_target_pairs={{0,1},{1,0},{2,3},{3,2},{4,5},{5,4},{6,7},{7,6},{8,9},{9,8},{10,11... | collective-permute-start | bytes 196616 | tf_op jit(solution)/shard_map/ppermute | solution.py:33
  21.6 11.3 %collective-permute-start.9 = (f32[64,256]{1,0:T(8,128)S(1)}, f32[64,256]{1,0:T(8,128)S(1)}, u32[]{:S(2)}, u32[]{:S(2)}) collective-permute-start(f32[64,256]{1,0:T(8,128)S(1)} %shard_map.115.refs_1_), channel_id=1, source_target_pairs={{0,2},{1,3},{2,0},{3,1},{4,6},{5,7},{6,4},{7,5},{8,10},{9,11},{10,... | collective-permute-start | bytes 196616 | tf_op jit(solution)/shard_map/ppermute | solution.py:33
  25.4 8.0 %collective-permute-start.13 = (f32[64,256]{1,0:T(8,128)S(1)}, f32[64,256]{1,0:T(8,128)S(1)}, u32[]{:S(2)}, u32[]{:S(2)}) collective-permute-start(f32[64,256]{1,0:T(8,128)S(1)} %shard_map.115.refs_1_), channel_id=1, source_target_pairs={{0,3},{1,2},{2,1},{3,0},{4,7},{5,6},{6,5},{7,4},{8,11},{9,10},{10,... | collective-permute-start | bytes 196616 | tf_op jit(solution)/shard_map/ppermute | solution.py:33
  27.3 6.1 %collective-permute-start.12 = (f32[64,256]{1,0:T(8,128)S(1)}, f32[64,256]{1,0:T(8,128)S(1)}, u32[]{:S(2)}, u32[]{:S(2)}) collective-permute-start(f32[64,256]{1,0:T(8,128)S(1)} %shard_map.115.refs_1_), channel_id=1, source_target_pairs={{0,1},{1,0},{2,3},{3,2},{4,5},{5,4},{6,7},{7,6},{8,9},{9,8},{10,11... | collective-permute-start | bytes 196616 | tf_op jit(solution)/shard_map/ppermute | solution.py:33
  29.2 8.8 %collective-permute-start.11 = (f32[64,256]{1,0:T(8,128)S(1)}, f32[64,256]{1,0:T(8,128)S(1)}, u32[]{:S(2)}, u32[]{:S(2)}) collective-permute-start(f32[64,256]{1,0:T(8,128)S(1)} %get-tuple-element.56), channel_id=1, source_target_pairs={{0,2},{1,3},{2,0},{3,1},{4,6},{5,7},{6,4},{7,5},{8,10},{9,11},{10,... | collective-permute-start | bytes 196616 | tf_op jit(solution)/shard_map/ppermute | solution.py:33
  31.1 7.6 %collective-permute-start.14 = (f32[64,256]{1,0:T(8,128)S(1)}, f32[64,256]{1,0:T(8,128)S(1)}, u32[]{:S(2)}, u32[]{:S(2)}) collective-permute-start(f32[64,256]{1,0:T(8,128)S(1)} %get-tuple-element.56), channel_id=1, source_target_pairs={{0,3},{1,2},{2,1},{3,0},{4,7},{5,6},{6,5},{7,4},{8,11},{9,10},{10,... | collective-permute-start | bytes 196616 | tf_op jit(solution)/shard_map/ppermute | solution.py:33
  32.8 5.9 %collective-permute-start.10 = (f32[64,256]{1,0:T(8,128)S(1)}, f32[64,256]{1,0:T(8,128)S(1)}, u32[]{:S(2)}, u32[]{:S(2)}) collective-permute-start(f32[64,256]{1,0:T(8,128)S(1)} %get-tuple-element.56), channel_id=1, source_target_pairs={{0,1},{1,0},{2,3},{3,2},{4,5},{5,4},{6,7},{7,6},{8,9},{9,8},{10,11... | collective-permute-start | bytes 196616 | tf_op jit(solution)/shard_map/ppermute | solution.py:33
  34.1 10.1 %collective-permute-start.16 = (f32[64,256]{1,0:T(8,128)S(1)}, f32[64,256]{1,0:T(8,128)S(1)}, u32[]{:S(2)}, u32[]{:S(2)}) collective-permute-start(f32[64,256]{1,0:T(8,128)S(1)} %get-tuple-element.59), channel_id=1, source_target_pairs={{0,2},{1,3},{2,0},{3,1},{4,6},{5,7},{6,4},{7,5},{8,10},{9,11},{10,... | collective-permute-start | bytes 196616 | tf_op jit(solution)/shard_map/ppermute | solution.py:33
  36.3 8.1 %collective-permute-start.17 = (f32[64,256]{1,0:T(8,128)S(1)}, f32[64,256]{1,0:T(8,128)S(1)}, u32[]{:S(2)}, u32[]{:S(2)}) collective-permute-start(f32[64,256]{1,0:T(8,128)S(1)} %get-tuple-element.59), channel_id=1, source_target_pairs={{0,3},{1,2},{2,1},{3,0},{4,7},{5,6},{6,5},{7,4},{8,11},{9,10},{10,... | collective-permute-start | bytes 196616 | tf_op jit(solution)/shard_map/ppermute | solution.py:33
  38.0 6.4 %collective-permute-start.15 = (f32[64,256]{1,0:T(8,128)S(1)}, f32[64,256]{1,0:T(8,128)S(1)}, u32[]{:S(2)}, u32[]{:S(2)}) collective-permute-start(f32[64,256]{1,0:T(8,128)S(1)} %get-tuple-element.59), channel_id=1, source_target_pairs={{0,1},{1,0},{2,3},{3,2},{4,5},{5,4},{6,7},{7,6},{8,9},{9,8},{10,11... | collective-permute-start | bytes 196616 | tf_op jit(solution)/shard_map/ppermute | solution.py:33
  39.4 9.9 %collective-permute-start.19 = (f32[64,256]{1,0:T(8,128)S(1)}, f32[64,256]{1,0:T(8,128)S(1)}, u32[]{:S(2)}, u32[]{:S(2)}) collective-permute-start(f32[64,256]{1,0:T(8,128)S(1)} %get-tuple-element.61.refs_2_), channel_id=1, source_target_pairs={{0,2},{1,3},{2,0},{3,1},{4,6},{5,7},{6,4},{7,5},{8,10},{9,11},{10,... | collective-permute-start | bytes 196616 | tf_op jit(solution)/shard_map/ppermute | solution.py:33
  41.5 8.1 %collective-permute-start.20 = (f32[64,256]{1,0:T(8,128)S(1)}, f32[64,256]{1,0:T(8,128)S(1)}, u32[]{:S(2)}, u32[]{:S(2)}) collective-permute-start(f32[64,256]{1,0:T(8,128)S(1)} %get-tuple-element.61.refs_2_), channel_id=1, source_target_pairs={{0,3},{1,2},{2,1},{3,0},{4,7},{5,6},{6,5},{7,4},{8,11},{9,10},{10,... | collective-permute-start | bytes 196616 | tf_op jit(solution)/shard_map/ppermute | solution.py:33
  44.2 5.4 %collective-permute-start.18 = (f32[64,256]{1,0:T(8,128)S(1)}, f32[64,256]{1,0:T(8,128)S(1)}, u32[]{:S(2)}, u32[]{:S(2)}) collective-permute-start(f32[64,256]{1,0:T(8,128)S(1)} %get-tuple-element.61.refs_2_), channel_id=1, source_target_pairs={{0,1},{1,0},{2,3},{3,2},{4,5},{5,4},{6,7},{7,6},{8,9},{9,8},{10,11... | collective-permute-start | bytes 196616 | tf_op jit(solution)/shard_map/ppermute | solution.py:33
  45.1 9.5 %collective-permute-start.21 = (f32[64,256]{1,0:T(8,128)S(1)}, f32[64,256]{1,0:T(8,128)S(1)}, u32[]{:S(2)}, u32[]{:S(2)}) collective-permute-start(f32[64,256]{1,0:T(8,128)S(1)} %get-tuple-element.65.refs_3_), channel_id=1, source_target_pairs={{0,2},{1,3},{2,0},{3,1},{4,6},{5,7},{6,4},{7,5},{8,10},{9,11},{10,... | collective-permute-start | bytes 196616 | tf_op jit(solution)/shard_map/ppermute | solution.py:33
  48.8 7.0 %collective-permute-start.25 = (f32[64,256]{1,0:T(8,128)S(1)}, f32[64,256]{1,0:T(8,128)S(1)}, u32[]{:S(2)}, u32[]{:S(2)}) collective-permute-start(f32[64,256]{1,0:T(8,128)S(1)} %get-tuple-element.65.refs_3_), channel_id=1, source_target_pairs={{0,3},{1,2},{2,1},{3,0},{4,7},{5,6},{6,5},{7,4},{8,11},{9,10},{10,... | collective-permute-start | bytes 196616 | tf_op jit(solution)/shard_map/ppermute | solution.py:33
  49.4 6.5 %collective-permute-start.24 = (f32[64,256]{1,0:T(8,128)S(1)}, f32[64,256]{1,0:T(8,128)S(1)}, u32[]{:S(2)}, u32[]{:S(2)}) collective-permute-start(f32[64,256]{1,0:T(8,128)S(1)} %get-tuple-element.65.refs_3_), channel_id=1, source_target_pairs={{0,1},{1,0},{2,3},{3,2},{4,5},{5,4},{6,7},{7,6},{8,9},{9,8},{10,11... | collective-permute-start | bytes 196616 | tf_op jit(solution)/shard_map/ppermute | solution.py:33
  50.3 10.1 %collective-permute-start.23 = (f32[64,256]{1,0:T(8,128)S(1)}, f32[64,256]{1,0:T(8,128)S(1)}, u32[]{:S(2)}, u32[]{:S(2)}) collective-permute-start(f32[64,256]{1,0:T(8,128)S(1)} %get-tuple-element.64), channel_id=1, source_target_pairs={{0,2},{1,3},{2,0},{3,1},{4,6},{5,7},{6,4},{7,5},{8,10},{9,11},{10,... | collective-permute-start | bytes 196616 | tf_op jit(solution)/shard_map/ppermute | solution.py:33
  54.0 6.9 %collective-permute-start.26 = (f32[64,256]{1,0:T(8,128)S(1)}, f32[64,256]{1,0:T(8,128)S(1)}, u32[]{:S(2)}, u32[]{:S(2)}) collective-permute-start(f32[64,256]{1,0:T(8,128)S(1)} %get-tuple-element.64), channel_id=1, source_target_pairs={{0,3},{1,2},{2,1},{3,0},{4,7},{5,6},{6,5},{7,4},{8,11},{9,10},{10,... | collective-permute-start | bytes 196616 | tf_op jit(solution)/shard_map/ppermute | solution.py:33
  54.5 6.3 %collective-permute-start.22 = (f32[64,256]{1,0:T(8,128)S(1)}, f32[64,256]{1,0:T(8,128)S(1)}, u32[]{:S(2)}, u32[]{:S(2)}) collective-permute-start(f32[64,256]{1,0:T(8,128)S(1)} %get-tuple-element.64), channel_id=1, source_target_pairs={{0,1},{1,0},{2,3},{3,2},{4,5},{5,4},{6,7},{7,6},{8,9},{9,8},{10,11... | collective-permute-start | bytes 196616 | tf_op jit(solution)/shard_map/ppermute | solution.py:33
  56.6 10.2 %collective-permute-start.28 = (f32[64,256]{1,0:T(8,128)S(1)}, f32[64,256]{1,0:T(8,128)S(1)}, u32[]{:S(2)}, u32[]{:S(2)}) collective-permute-start(f32[64,256]{1,0:T(8,128)S(1)} %get-tuple-element.67), channel_id=1, source_target_pairs={{0,2},{1,3},{2,0},{3,1},{4,6},{5,7},{6,4},{7,5},{8,10},{9,11},{10,... | collective-permute-start | bytes 196616 | tf_op jit(solution)/shard_map/ppermute | solution.py:33
  59.5 7.6 %collective-permute-start.29 = (f32[64,256]{1,0:T(8,128)S(1)}, f32[64,256]{1,0:T(8,128)S(1)}, u32[]{:S(2)}, u32[]{:S(2)}) collective-permute-start(f32[64,256]{1,0:T(8,128)S(1)} %get-tuple-element.67), channel_id=1, source_target_pairs={{0,3},{1,2},{2,1},{3,0},{4,7},{5,6},{6,5},{7,4},{8,11},{9,10},{10,... | collective-permute-start | bytes 196616 | tf_op jit(solution)/shard_map/ppermute | solution.py:33
  60.4 6.7 %collective-permute-start.27 = (f32[64,256]{1,0:T(8,128)S(1)}, f32[64,256]{1,0:T(8,128)S(1)}, u32[]{:S(2)}, u32[]{:S(2)}) collective-permute-start(f32[64,256]{1,0:T(8,128)S(1)} %get-tuple-element.67), channel_id=1, source_target_pairs={{0,1},{1,0},{2,3},{3,2},{4,5},{5,4},{6,7},{7,6},{8,9},{9,8},{10,11... | collective-permute-start | bytes 196616 | tf_op jit(solution)/shard_map/ppermute | solution.py:33
  61.5 10.3 %collective-permute-start.31 = (f32[64,256]{1,0:T(8,128)S(1)}, f32[64,256]{1,0:T(8,128)S(1)}, u32[]{:S(2)}, u32[]{:S(2)}) collective-permute-start(f32[64,256]{1,0:T(8,128)S(1)} %get-tuple-element.69.refs_4_), channel_id=1, source_target_pairs={{0,2},{1,3},{2,0},{3,1},{4,6},{5,7},{6,4},{7,5},{8,10},{9,11},{10,... | collective-permute-start | bytes 196616 | tf_op jit(solution)/shard_map/ppermute | solution.py:33
  64.6 7.8 %collective-permute-start.32 = (f32[64,256]{1,0:T(8,128)S(1)}, f32[64,256]{1,0:T(8,128)S(1)}, u32[]{:S(2)}, u32[]{:S(2)}) collective-permute-start(f32[64,256]{1,0:T(8,128)S(1)} %get-tuple-element.69.refs_4_), channel_id=1, source_target_pairs={{0,3},{1,2},{2,1},{3,0},{4,7},{5,6},{6,5},{7,4},{8,11},{9,10},{10,... | collective-permute-start | bytes 196616 | tf_op jit(solution)/shard_map/ppermute | solution.py:33
  66.7 5.7 %collective-permute-start.30 = (f32[64,256]{1,0:T(8,128)S(1)}, f32[64,256]{1,0:T(8,128)S(1)}, u32[]{:S(2)}, u32[]{:S(2)}) collective-permute-start(f32[64,256]{1,0:T(8,128)S(1)} %get-tuple-element.69.refs_4_), channel_id=1, source_target_pairs={{0,1},{1,0},{2,3},{3,2},{4,5},{5,4},{6,7},{7,6},{8,9},{9,8},{10,11... | collective-permute-start | bytes 196616 | tf_op jit(solution)/shard_map/ppermute | solution.py:33
  67.8 10.3 %collective-permute-start.33 = (f32[64,256]{1,0:T(8,128)S(1)}, f32[64,256]{1,0:T(8,128)S(1)}, u32[]{:S(2)}, u32[]{:S(2)}) collective-permute-start(f32[64,256]{1,0:T(8,128)S(1)} %get-tuple-element.73.refs_5_), channel_id=1, source_target_pairs={{0,2},{1,3},{2,0},{3,1},{4,6},{5,7},{6,4},{7,5},{8,10},{9,11},{10,... | collective-permute-start | bytes 196616 | tf_op jit(solution)/shard_map/ppermute | solution.py:33
  71.3 7.1 %collective-permute-start.37 = (f32[64,256]{1,0:T(8,128)S(1)}, f32[64,256]{1,0:T(8,128)S(1)}, u32[]{:S(2)}, u32[]{:S(2)}) collective-permute-start(f32[64,256]{1,0:T(8,128)S(1)} %get-tuple-element.73.refs_5_), channel_id=1, source_target_pairs={{0,3},{1,2},{2,1},{3,0},{4,7},{5,6},{6,5},{7,4},{8,11},{9,10},{10,... | collective-permute-start | bytes 196616 | tf_op jit(solution)/shard_map/ppermute | solution.py:33
  71.9 6.5 %collective-permute-start.36 = (f32[64,256]{1,0:T(8,128)S(1)}, f32[64,256]{1,0:T(8,128)S(1)}, u32[]{:S(2)}, u32[]{:S(2)}) collective-permute-start(f32[64,256]{1,0:T(8,128)S(1)} %get-tuple-element.73.refs_5_), channel_id=1, source_target_pairs={{0,1},{1,0},{2,3},{3,2},{4,5},{5,4},{6,7},{7,6},{8,9},{9,8},{10,11... | collective-permute-start | bytes 196616 | tf_op jit(solution)/shard_map/ppermute | solution.py:33
  73.1 10.1 %collective-permute-start.35 = (f32[64,256]{1,0:T(8,128)S(1)}, f32[64,256]{1,0:T(8,128)S(1)}, u32[]{:S(2)}, u32[]{:S(2)}) collective-permute-start(f32[64,256]{1,0:T(8,128)S(1)} %get-tuple-element.72), channel_id=1, source_target_pairs={{0,2},{1,3},{2,0},{3,1},{4,6},{5,7},{6,4},{7,5},{8,10},{9,11},{10,... | collective-permute-start | bytes 196616 | tf_op jit(solution)/shard_map/ppermute | solution.py:33
  76.5 7.0 %collective-permute-start.38 = (f32[64,256]{1,0:T(8,128)S(1)}, f32[64,256]{1,0:T(8,128)S(1)}, u32[]{:S(2)}, u32[]{:S(2)}) collective-permute-start(f32[64,256]{1,0:T(8,128)S(1)} %get-tuple-element.72), channel_id=1, source_target_pairs={{0,3},{1,2},{2,1},{3,0},{4,7},{5,6},{6,5},{7,4},{8,11},{9,10},{10,... | collective-permute-start | bytes 196616 | tf_op jit(solution)/shard_map/ppermute | solution.py:33
  78.0 5.4 %collective-permute-start.34 = (f32[64,256]{1,0:T(8,128)S(1)}, f32[64,256]{1,0:T(8,128)S(1)}, u32[]{:S(2)}, u32[]{:S(2)}) collective-permute-start(f32[64,256]{1,0:T(8,128)S(1)} %get-tuple-element.72), channel_id=1, source_target_pairs={{0,1},{1,0},{2,3},{3,2},{4,5},{5,4},{6,7},{7,6},{8,9},{9,8},{10,11... | collective-permute-start | bytes 196616 | tf_op jit(solution)/shard_map/ppermute | solution.py:33
  79.1 10.2 %collective-permute-start.40 = (f32[64,256]{1,0:T(8,128)S(1)}, f32[64,256]{1,0:T(8,128)S(1)}, u32[]{:S(2)}, u32[]{:S(2)}) collective-permute-start(f32[64,256]{1,0:T(8,128)S(1)} %get-tuple-element.75), channel_id=1, source_target_pairs={{0,2},{1,3},{2,0},{3,1},{4,6},{5,7},{6,4},{7,5},{8,10},{9,11},{10,... | collective-permute-start | bytes 196616 | tf_op jit(solution)/shard_map/ppermute | solution.py:33
  82.0 7.6 %collective-permute-start.41 = (f32[64,256]{1,0:T(8,128)S(1)}, f32[64,256]{1,0:T(8,128)S(1)}, u32[]{:S(2)}, u32[]{:S(2)}) collective-permute-start(f32[64,256]{1,0:T(8,128)S(1)} %get-tuple-element.75), channel_id=1, source_target_pairs={{0,3},{1,2},{2,1},{3,0},{4,7},{5,6},{6,5},{7,4},{8,11},{9,10},{10,... | collective-permute-start | bytes 196616 | tf_op jit(solution)/shard_map/ppermute | solution.py:33
  83.2 6.3 %collective-permute-start.39 = (f32[64,256]{1,0:T(8,128)S(1)}, f32[64,256]{1,0:T(8,128)S(1)}, u32[]{:S(2)}, u32[]{:S(2)}) collective-permute-start(f32[64,256]{1,0:T(8,128)S(1)} %get-tuple-element.75), channel_id=1, source_target_pairs={{0,1},{1,0},{2,3},{3,2},{4,5},{5,4},{6,7},{7,6},{8,9},{9,8},{10,11... | collective-permute-start | bytes 196616 | tf_op jit(solution)/shard_map/ppermute | solution.py:33
  84.2 10.3 %collective-permute-start.43 = (f32[64,256]{1,0:T(8,128)S(1)}, f32[64,256]{1,0:T(8,128)S(1)}, u32[]{:S(2)}, u32[]{:S(2)}) collective-permute-start(f32[64,256]{1,0:T(8,128)S(1)} %get-tuple-element.77.refs_6_), channel_id=1, source_target_pairs={{0,2},{1,3},{2,0},{3,1},{4,6},{5,7},{6,4},{7,5},{8,10},{9,11},{10,... | collective-permute-start | bytes 196616 | tf_op jit(solution)/shard_map/ppermute | solution.py:33
  87.2 7.6 %collective-permute-start.44 = (f32[64,256]{1,0:T(8,128)S(1)}, f32[64,256]{1,0:T(8,128)S(1)}, u32[]{:S(2)}, u32[]{:S(2)}) collective-permute-start(f32[64,256]{1,0:T(8,128)S(1)} %get-tuple-element.77.refs_6_), channel_id=1, source_target_pairs={{0,3},{1,2},{2,1},{3,0},{4,7},{5,6},{6,5},{7,4},{8,11},{9,10},{10,... | collective-permute-start | bytes 196616 | tf_op jit(solution)/shard_map/ppermute | solution.py:33
  89.3 5.4 %collective-permute-start.42 = (f32[64,256]{1,0:T(8,128)S(1)}, f32[64,256]{1,0:T(8,128)S(1)}, u32[]{:S(2)}, u32[]{:S(2)}) collective-permute-start(f32[64,256]{1,0:T(8,128)S(1)} %get-tuple-element.77.refs_6_), channel_id=1, source_target_pairs={{0,1},{1,0},{2,3},{3,2},{4,5},{5,4},{6,7},{7,6},{8,9},{9,8},{10,11... | collective-permute-start | bytes 196616 | tf_op jit(solution)/shard_map/ppermute | solution.py:33
  90.3 5.9 %collective-permute-start.46 = (f32[64,256]{1,0:T(8,128)S(1)}, f32[64,256]{1,0:T(8,128)S(1)}, u32[]{:S(2)}, u32[]{:S(2)}) collective-permute-start(f32[64,256]{1,0:T(8,128)S(1)} %get-tuple-element.79.refs_7_), channel_id=1, source_target_pairs={{0,2},{1,3},{2,0},{3,1},{4,6},{5,7},{6,4},{7,5},{8,10},{9,11},{10,... | collective-permute-start | bytes 196616 | tf_op jit(solution)/shard_map/ppermute | solution.py:33
  93.9 6.1 %collective-permute-start.47 = (f32[64,256]{1,0:T(8,128)S(1)}, f32[64,256]{1,0:T(8,128)S(1)}, u32[]{:S(2)}, u32[]{:S(2)}) collective-permute-start(f32[64,256]{1,0:T(8,128)S(1)} %get-tuple-element.79.refs_7_), channel_id=1, source_target_pairs={{0,3},{1,2},{2,1},{3,0},{4,7},{5,6},{6,5},{7,4},{8,11},{9,10},{10,... | collective-permute-start | bytes 196616 | tf_op jit(solution)/shard_map/ppermute | solution.py:33
  94.5 4.3 %collective-permute-start.45 = (f32[64,256]{1,0:T(8,128)S(1)}, f32[64,256]{1,0:T(8,128)S(1)}, u32[]{:S(2)}, u32[]{:S(2)}) collective-permute-start(f32[64,256]{1,0:T(8,128)S(1)} %get-tuple-element.79.refs_7_), channel_id=1, source_target_pairs={{0,1},{1,0},{2,3},{3,2},{4,5},{5,4},{6,7},{7,6},{8,9},{9,8},{10,11... | collective-permute-start | bytes 196616 | tf_op jit(solution)/shard_map/ppermute | solution.py:33
  96.1 17.7 %copy-start.1 = (f32[2,256,1024]{2,1,0:T(8,128)S(1)}, f32[2,256,1024]{2,1,0:T(8,128)}, u32[]{:S(2)}) copy-start(f32[2,256,1024]{2,1,0:T(8,128)} %refs_0_.1) | copy-start | bytes 6291460
  96.2 17.7 %copy-start.4 = (f32[1,256,1024]{2,1,0:T(8,128)S(1)}, f32[1,256,1024]{2,1,0:T(8,128)}, u32[]{:S(2)}) copy-start(f32[1,256,1024]{2,1,0:T(8,128)} %refs_1_.1) | copy-start | bytes 3145732
  101.2 1.4 %collective-permute-start.48 = (f32[4,16,512]{2,1,0:T(8,128)S(1)}, f32[4,16,512]{2,1,0:T(8,128)S(1)}, u32[]{:S(2)}, u32[]{:S(2)}) collective-permute-start(f32[4,16,512]{2,1,0:T(8,128)S(1)} %get-tuple-element.83), channel_id=1, source_target_pairs={{0,4},{4,0},{8,12},{12,8},{16,20},{20,16},{24,28},{28,24},{1,5},{5... | collective-permute-start | bytes 393224 | tf_op jit(solution)/shard_map/ppermute | solution.py:281
  102.6 5.3 %collective-permute-start.49 = (f32[2,16,512]{2,1,0:T(8,128)S(1)}, f32[2,16,512]{2,1,0:T(8,128)S(1)}, u32[]{:S(2)}, u32[]{:S(2)}) collective-permute-start(f32[2,16,512]{2,1,0:T(8,128)S(1)} %get-tuple-element.85), channel_id=1, source_target_pairs={{0,24},{4,28},{8,16},{12,20},{16,8},{20,12},{24,0},{28,4},{1,25},{... | collective-permute-start | bytes 196616 | tf_op jit(solution)/shard_map/ppermute | solution.py:81
  105.1 4.3 %collective-permute-start.50 = (f32[2,16,512]{2,1,0:T(8,128)S(1)}, f32[2,16,512]{2,1,0:T(8,128)S(1)}, u32[]{:S(2)}, u32[]{:S(2)}) collective-permute-start(f32[2,16,512]{2,1,0:T(8,128)S(1)} %get-tuple-element.86), channel_id=1, source_target_pairs={{0,16},{4,20},{8,24},{12,28},{16,0},{20,4},{24,8},{28,12},{1,17},{... | collective-permute-start | bytes 196616 | tf_op jit(solution)/shard_map/ppermute | solution.py:81
  105.6 4.3 %collective-permute-start.51 = (f32[2,16,512]{2,1,0:T(8,128)S(1)}, f32[2,16,512]{2,1,0:T(8,128)S(1)}, u32[]{:S(2)}, u32[]{:S(2)}) collective-permute-start(f32[2,16,512]{2,1,0:T(8,128)S(1)} %get-tuple-element.87), channel_id=1, source_target_pairs={{0,8},{4,12},{8,0},{12,4},{16,24},{20,28},{24,16},{28,20},{1,9},{5... | collective-permute-start | bytes 196616 | tf_op jit(solution)/shard_map/ppermute | solution.py:81
  110.3 5.8 %collective-permute-start.52 = (f32[16,1024]{1,0:T(8,128)S(1)}, f32[16,1024]{1,0:T(8,128)S(1)}, u32[]{:S(2)}, u32[]{:S(2)}) collective-permute-start(f32[16,1024]{1,0:T(8,128)S(1)} %get-tuple-element.89.refs_2_.refs_0_), channel_id=1, source_target_pairs={{0,2},{1,3},{2,0},{3,1},{4,6},{5,7},{6,4},{7,5},{8,10},{9,11},{10,... | collective-permute-start | bytes 196616 | tf_op jit(solution)/shard_map/ppermute | solution.py:33
  111.7 6.1 %collective-permute-start.53 = (f32[16,1024]{1,0:T(8,128)S(1)}, f32[16,1024]{1,0:T(8,128)S(1)}, u32[]{:S(2)}, u32[]{:S(2)}) collective-permute-start(f32[16,1024]{1,0:T(8,128)S(1)} %get-tuple-element.89.refs_2_.refs_0_), channel_id=1, source_target_pairs={{0,3},{1,2},{2,1},{3,0},{4,7},{5,6},{6,5},{7,4},{8,11},{9,10},{10,... | collective-permute-start | bytes 196616 | tf_op jit(solution)/shard_map/ppermute | solution.py:33
  112.5 5.2 %collective-permute-start.54 = (f32[16,1024]{1,0:T(8,128)S(1)}, f32[16,1024]{1,0:T(8,128)S(1)}, u32[]{:S(2)}, u32[]{:S(2)}) collective-permute-start(f32[16,1024]{1,0:T(8,128)S(1)} %get-tuple-element.89.refs_2_.refs_0_), channel_id=1, source_target_pairs={{0,1},{1,0},{2,3},{3,2},{4,5},{5,4},{6,7},{7,6},{8,9},{9,8},{10,11... | collective-permute-start | bytes 196616 | tf_op jit(solution)/shard_map/ppermute | solution.py:33
  118.1 5.2 %collective-permute-start.55 = (f32[16,512]{1,0:T(8,128)S(1)}, f32[16,512]{1,0:T(8,128)S(1)}, u32[]{:S(2)}, u32[]{:S(2)}) collective-permute-start(f32[16,512]{1,0:T(8,128)S(1)} %get-tuple-element.97), channel_id=1, source_target_pairs={{0,2},{1,3},{2,0},{3,1},{4,6},{5,7},{6,4},{7,5},{8,10},{9,11},{10,... | collective-permute-start | bytes 98312 | tf_op jit(solution)/shard_map/ppermute | solution.py:33
  119.5 5.7 %collective-permute-start.56 = (f32[16,512]{1,0:T(8,128)S(1)}, f32[16,512]{1,0:T(8,128)S(1)}, u32[]{:S(2)}, u32[]{:S(2)}) collective-permute-start(f32[16,512]{1,0:T(8,128)S(1)} %get-tuple-element.98), channel_id=1, source_target_pairs={{0,3},{1,2},{2,1},{3,0},{4,7},{5,6},{6,5},{7,4},{8,11},{9,10},{10,... | collective-permute-start | bytes 98312 | tf_op jit(solution)/shard_map/ppermute | solution.py:33
  120.9 4.4 %collective-permute-start.57 = (f32[16,512]{1,0:T(8,128)S(1)}, f32[16,512]{1,0:T(8,128)S(1)}, u32[]{:S(2)}, u32[]{:S(2)}) collective-permute-start(f32[16,512]{1,0:T(8,128)S(1)} %get-tuple-element.99), channel_id=1, source_target_pairs={{0,1},{1,0},{2,3},{3,2},{4,5},{5,4},{6,7},{7,6},{8,9},{9,8},{10,11... | collective-permute-start | bytes 98312 | tf_op jit(solution)/shard_map/ppermute | solution.py:33
  125.6 4.7 %collective-permute-start.58 = (f32[16,256]{1,0:T(8,128)S(1)}, f32[16,256]{1,0:T(8,128)S(1)}, u32[]{:S(2)}, u32[]{:S(2)}) collective-permute-start(f32[16,256]{1,0:T(8,128)S(1)} %shard_map.124.refs_0_), channel_id=1, source_target_pairs={{0,2},{1,3},{2,0},{3,1},{4,6},{5,7},{6,4},{7,5},{8,10},{9,11},{10,... | collective-permute-start | bytes 49160 | tf_op jit(solution)/shard_map/ppermute | solution.py:33
  126.9 5.5 %collective-permute-start.59 = (f32[16,256]{1,0:T(8,128)S(1)}, f32[16,256]{1,0:T(8,128)S(1)}, u32[]{:S(2)}, u32[]{:S(2)}) collective-permute-start(f32[16,256]{1,0:T(8,128)S(1)} %shard_map.124.refs_0_), channel_id=1, source_target_pairs={{0,3},{1,2},{2,1},{3,0},{4,7},{5,6},{6,5},{7,4},{8,11},{9,10},{10,... | collective-permute-start | bytes 49160 | tf_op jit(solution)/shard_map/ppermute | solution.py:33
  128.3 4.2 %collective-permute-start.60 = (f32[16,256]{1,0:T(8,128)S(1)}, f32[16,256]{1,0:T(8,128)S(1)}, u32[]{:S(2)}, u32[]{:S(2)}) collective-permute-start(f32[16,256]{1,0:T(8,128)S(1)} %shard_map.124.refs_0_), channel_id=1, source_target_pairs={{0,1},{1,0},{2,3},{3,2},{4,5},{5,4},{6,7},{7,6},{8,9},{9,8},{10,11... | collective-permute-start | bytes 49160 | tf_op jit(solution)/shard_map/ppermute | solution.py:33
  (7 other events, 93.3 us)

commit v27 on v22

--- a/solution.py
+++ b/solution.py
@@ -40,7 +40,7 @@
     pieces = [(me * rows, value)]
     distances = list(range(1, members))
     if far_first:
-        distances = distances[1:] + distances[:1]
+        distances = distances[::-1]
     for distance in distances:
         owner = partner(me, distance, members)
         tied = value
@@ -403,7 +403,7 @@
             total = total + ref[:, rows:]
         if width > rows:
             refs[members + 4][...] = total
-        pieces = [ref[:, :rows] for ref in held[-1:] + held[:-1]]
+        pieces = [ref[:, :rows] for ref in held[::-1]]
         put_in_order([own_ref[...]] + pieces, whole)
         out[...] = total[:, :rows] - split_product(whole[...], top_ref[0], rest_ref[0])
 
@@ -439,7 +439,7 @@
         out, whole = refs[-2:]
         held = [refs[d][...] for d in range(members)]
         if far_first:
-            held = held[:1] + held[-1:] + held[1:-1] if members > 2 else held
+            held = held[:1] + held[:0:-1]
         put_in_order(held, whole)
         result = split_product(whole[...], top_ref[index], rest_ref[index])
         if others is not None:
@@ -529,7 +529,7 @@
     shares = share_out(
         received, jnp.swapaxes(rhs_anc, 1, 2), order, slots, tile_rows, tie
     )
-    far_first = list(range(2, members)) + list(range(1, min(members, 2)))
+    far_first = list(range(members - 1, 0, -1))
     first_share, others = shares[0], shares[1:]
     sums = [first_share] + [send(first_share, "grp", d) for d in far_first]
     inverse_top, inverse_rest, below_top, below_rest = split_factors(

time: 134 us -> 134 us (level)
  starting transfers between devices: 90.2 us -> 92.9 us
  waiting for transfers between devices: 22.9 us -> 20.7 us
    ppermute x57, starting transfers between devices: 86.6 us -> 89.3 us  [send(): return lax.ppermute(value, axis, pairs)]
    ppermute x57, waiting for transfers between devices: 18.9 us -> 16.6 us  [send(): return lax.ppermute(value, axis, pairs)]
where the time goes in v27:
time: 134 us
  starting transfers between devices  92.9 us (69%)
  waiting for transfers between devices  20.7 us (15%)
  Pallas kernels  7.54 us (6%)
  matrix products  7.53 us (6%)
  between operations  2.07 us (2%)
  local copies, waits for them, and re-layouts  1.85 us (1%)
  other arithmetic  1.41 us (1%)
    ppermute x57, starting transfers between devices, send(): return lax.ppermute(value, axis, pairs)  89.3 us
    ppermute x57, waiting for transfers between devices, send(): return lax.ppermute(value, axis, pairs)  16.6 us
    pallas_call x13, Pallas kernels, local_kernel(): pl.pallas_call(body, out_shape=list(outs), in_specs=specs or [VMEM] * len...  7.54 us
    dot_general x12, matrix products, contract_last(): lax.dot_general(left, right, (((left.ndim - 1,), (right.ndim - 1,)), ((),...  7.53 us
    ppermute x3, starting transfers between devices, swap(): return lax.ppermute(value, axis, pairs)  3.55 us
    ppermute x3, waiting for transfers between devices, swap(): return lax.ppermute(value, axis, pairs)  2.74 us
  transfers between devices with their start and end apart: 61, of which 18 were waited for; matrix products, arithmetic and copies ran while one was open for 7% of the time, Pallas kernels for 3%

profile of v27, /device:TPU:0, one launch (start us, length us, event | category | flops | bytes accessed | tf_op | source)
XLA Modules:
  0.0 134.0 jit_solution(3974903380456861908)
XLA Ops:
  0.6 1.0 copy-done.2
  1.9 3.1 %collective-permute-start = (f32[64,256]{1,0:T(8,128)S(1)}, f32[64,256]{1,0:T(8,128)S(1)}, u32[]{:S(2)}, u32[]{:S(2)}) collective-permute-start(f32[64,256]{1,0:T(8,128)S(1)} %get-tuple-element.52.refs_0_), channel_id=1, source_target_pairs={{0,1},{1,0},{2,3},{3,2},{4,5},{5,4},{6,7},{7,6},{8,9},{9,8},{10,11... | collective-permute-start | bytes 196616 | tf_op jit(solution)/shard_map/ppermute | solution.py:33
  5.0 2.6 %collective-permute-start.1 = (f32[64,256]{1,0:T(8,128)S(1)}, f32[64,256]{1,0:T(8,128)S(1)}, u32[]{:S(2)}, u32[]{:S(2)}) collective-permute-start(f32[64,256]{1,0:T(8,128)S(1)} %get-tuple-element.52.refs_0_), channel_id=1, source_target_pairs={{0,2},{1,3},{2,0},{3,1},{4,6},{5,7},{6,4},{7,5},{8,10},{9,11},{10,... | collective-permute-start | bytes 196616 | tf_op jit(solution)/shard_map/ppermute | solution.py:33
  7.6 0.9 collective-permute-start.3
  8.5 3.5 %collective-permute-start.4 = (f32[64,256]{1,0:T(8,128)S(1)}, f32[64,256]{1,0:T(8,128)S(1)}, u32[]{:S(2)}, u32[]{:S(2)}) collective-permute-start(f32[64,256]{1,0:T(8,128)S(1)} %get-tuple-element.53.refs_0_), channel_id=1, source_target_pairs={{0,2},{1,3},{2,0},{3,1},{4,6},{5,7},{6,4},{7,5},{8,10},{9,11},{10,... | collective-permute-start | bytes 196616 | tf_op jit(solution)/shard_map/ppermute | solution.py:33
  12.0 1.4 %fusion = (bf16[1,256,1024]{2,1,0:T(8,128)(2,1)S(1)}, bf16[1,256,1024]{2,1,0:T(8,128)(2,1)S(1)}) fusion(f32[1,4,256,1024]{3,2,1,0:T(8,128)} %param.11), kind=kLoop, calls=%fused_computation.2 | loop fusion | flops 1048576 | bytes 2097152 | tf_op jit(solution)/shard_map/convert_element_type | solution.py:487
  14.6 3.0 %collective-permute-start.6 = (f32[64,256]{1,0:T(8,128)S(1)}, f32[64,256]{1,0:T(8,128)S(1)}, u32[]{:S(2)}, u32[]{:S(2)}) collective-permute-start(f32[64,256]{1,0:T(8,128)S(1)} %shard_map.114.refs_0_), channel_id=1, source_target_pairs={{0,1},{1,0},{2,3},{3,2},{4,5},{5,4},{6,7},{7,6},{8,9},{9,8},{10,11... | collective-permute-start | bytes 196616 | tf_op jit(solution)/shard_map/ppermute | solution.py:33
  17.7 2.1 %collective-permute-start.7 = (f32[64,256]{1,0:T(8,128)S(1)}, f32[64,256]{1,0:T(8,128)S(1)}, u32[]{:S(2)}, u32[]{:S(2)}) collective-permute-start(f32[64,256]{1,0:T(8,128)S(1)} %shard_map.114.refs_0_), channel_id=1, source_target_pairs={{0,2},{1,3},{2,0},{3,1},{4,6},{5,7},{6,4},{7,5},{8,10},{9,11},{10,... | collective-permute-start | bytes 196616 | tf_op jit(solution)/shard_map/ppermute | solution.py:33
  19.8 1.4 %collective-permute-start.8 = (f32[64,256]{1,0:T(8,128)S(1)}, f32[64,256]{1,0:T(8,128)S(1)}, u32[]{:S(2)}, u32[]{:S(2)}) collective-permute-start(f32[64,256]{1,0:T(8,128)S(1)} %shard_map.114.refs_0_), channel_id=1, source_target_pairs={{0,3},{1,2},{2,1},{3,0},{4,7},{5,6},{6,5},{7,4},{8,11},{9,10},{10,... | collective-permute-start | bytes 196616 | tf_op jit(solution)/shard_map/ppermute | solution.py:33
  21.7 2.3 %collective-permute-start.9 = (f32[64,256]{1,0:T(8,128)S(1)}, f32[64,256]{1,0:T(8,128)S(1)}, u32[]{:S(2)}, u32[]{:S(2)}) collective-permute-start(f32[64,256]{1,0:T(8,128)S(1)} %shard_map.115.refs_1_), channel_id=1, source_target_pairs={{0,2},{1,3},{2,0},{3,1},{4,6},{5,7},{6,4},{7,5},{8,10},{9,11},{10,... | collective-permute-start | bytes 196616 | tf_op jit(solution)/shard_map/ppermute | solution.py:33
  24.0 0.7 collective-permute-start.13
  24.8 3.1 %collective-permute-done.7 = f32[64,256]{1,0:T(8,128)S(1)} collective-permute-done((f32[64,256]{1,0:T(8,128)S(1)}, f32[64,256]{1,0:T(8,128)S(1)}, u32[]{:S(2)}, u32[]{:S(2)}) %collective-permute-start.7) | collective-permute-done | bytes 65568 | tf_op jit(solution)/shard_map/ppermute | solution.py:33
  28.4 0.6 constant_dynamic-update-slice_fusion.51
  29.0 3.9 %collective-permute-start.11 = (f32[64,256]{1,0:T(8,128)S(1)}, f32[64,256]{1,0:T(8,128)S(1)}, u32[]{:S(2)}, u32[]{:S(2)}) collective-permute-start(f32[64,256]{1,0:T(8,128)S(1)} %get-tuple-element.56), channel_id=1, source_target_pairs={{0,2},{1,3},{2,0},{3,1},{4,6},{5,7},{6,4},{7,5},{8,10},{9,11},{10,... | collective-permute-start | bytes 196616 | tf_op jit(solution)/shard_map/ppermute | solution.py:33
  33.6 0.6 constant_dynamic-update-slice_fusion.43
  34.2 3.8 %collective-permute-start.16 = (f32[64,256]{1,0:T(8,128)S(1)}, f32[64,256]{1,0:T(8,128)S(1)}, u32[]{:S(2)}, u32[]{:S(2)}) collective-permute-start(f32[64,256]{1,0:T(8,128)S(1)} %get-tuple-element.59), channel_id=1, source_target_pairs={{0,2},{1,3},{2,0},{3,1},{4,6},{5,7},{6,4},{7,5},{8,10},{9,11},{10,... | collective-permute-start | bytes 196616 | tf_op jit(solution)/shard_map/ppermute | solution.py:33
  38.7 1.0 collective-permute-done.14
  40.4 2.8 %collective-permute-start.19 = (f32[64,256]{1,0:T(8,128)S(1)}, f32[64,256]{1,0:T(8,128)S(1)}, u32[]{:S(2)}, u32[]{:S(2)}) collective-permute-start(f32[64,256]{1,0:T(8,128)S(1)} %get-tuple-element.61.refs_2_), channel_id=1, source_target_pairs={{0,2},{1,3},{2,0},{3,1},{4,6},{5,7},{6,4},{7,5},{8,10},{9,11},{10,... | collective-permute-start | bytes 196616 | tf_op jit(solution)/shard_map/ppermute | solution.py:33
  43.2 0.7 collective-permute-start.20
  44.4 0.6 constant_dynamic-update-slice_fusion.33
  45.0 4.0 %collective-permute-start.21 = (f32[64,256]{1,0:T(8,128)S(1)}, f32[64,256]{1,0:T(8,128)S(1)}, u32[]{:S(2)}, u32[]{:S(2)}) collective-permute-start(f32[64,256]{1,0:T(8,128)S(1)} %get-tuple-element.65.refs_3_), channel_id=1, source_target_pairs={{0,2},{1,3},{2,0},{3,1},{4,6},{5,7},{6,4},{7,5},{8,10},{9,11},{10,... | collective-permute-start | bytes 196616 | tf_op jit(solution)/shard_map/ppermute | solution.py:33
  49.0 1.9 %collective-permute-start.25 = (f32[64,256]{1,0:T(8,128)S(1)}, f32[64,256]{1,0:T(8,128)S(1)}, u32[]{:S(2)}, u32[]{:S(2)}) collective-permute-start(f32[64,256]{1,0:T(8,128)S(1)} %get-tuple-element.65.refs_3_), channel_id=1, source_target_pairs={{0,3},{1,2},{2,1},{3,0},{4,7},{5,6},{6,5},{7,4},{8,11},{9,10},{10,... | collective-permute-start | bytes 196616 | tf_op jit(solution)/shard_map/ppermute | solution.py:33
  51.0 0.6 constant_dynamic-update-slice_fusion.35
  51.6 2.5 %collective-permute-start.23 = (f32[64,256]{1,0:T(8,128)S(1)}, f32[64,256]{1,0:T(8,128)S(1)}, u32[]{:S(2)}, u32[]{:S(2)}) collective-permute-start(f32[64,256]{1,0:T(8,128)S(1)} %get-tuple-element.64), channel_id=1, source_target_pairs={{0,2},{1,3},{2,0},{3,1},{4,6},{5,7},{6,4},{7,5},{8,10},{9,11},{10,... | collective-permute-start | bytes 196616 | tf_op jit(solution)/shard_map/ppermute | solution.py:33
  54.2 1.9 %collective-permute-start.26 = (f32[64,256]{1,0:T(8,128)S(1)}, f32[64,256]{1,0:T(8,128)S(1)}, u32[]{:S(2)}, u32[]{:S(2)}) collective-permute-start(f32[64,256]{1,0:T(8,128)S(1)} %get-tuple-element.64), channel_id=1, source_target_pairs={{0,3},{1,2},{2,1},{3,0},{4,7},{5,6},{6,5},{7,4},{8,11},{9,10},{10,... | collective-permute-start | bytes 196616 | tf_op jit(solution)/shard_map/ppermute | solution.py:33
  56.8 3.6 %collective-permute-start.28 = (f32[64,256]{1,0:T(8,128)S(1)}, f32[64,256]{1,0:T(8,128)S(1)}, u32[]{:S(2)}, u32[]{:S(2)}) collective-permute-start(f32[64,256]{1,0:T(8,128)S(1)} %get-tuple-element.67), channel_id=1, source_target_pairs={{0,2},{1,3},{2,0},{3,1},{4,6},{5,7},{6,4},{7,5},{8,10},{9,11},{10,... | collective-permute-start | bytes 196616 | tf_op jit(solution)/shard_map/ppermute | solution.py:33
  60.4 0.8 collective-permute-start.29
  62.0 3.6 %collective-permute-start.31 = (f32[64,256]{1,0:T(8,128)S(1)}, f32[64,256]{1,0:T(8,128)S(1)}, u32[]{:S(2)}, u32[]{:S(2)}) collective-permute-start(f32[64,256]{1,0:T(8,128)S(1)} %get-tuple-element.69.refs_4_), channel_id=1, source_target_pairs={{0,2},{1,3},{2,0},{3,1},{4,6},{5,7},{6,4},{7,5},{8,10},{9,11},{10,... | collective-permute-start | bytes 196616 | tf_op jit(solution)/shard_map/ppermute | solution.py:33
  65.6 0.8 collective-permute-start.32
  67.6 4.0 %collective-permute-start.33 = (f32[64,256]{1,0:T(8,128)S(1)}, f32[64,256]{1,0:T(8,128)S(1)}, u32[]{:S(2)}, u32[]{:S(2)}) collective-permute-start(f32[64,256]{1,0:T(8,128)S(1)} %get-tuple-element.73.refs_5_), channel_id=1, source_target_pairs={{0,2},{1,3},{2,0},{3,1},{4,6},{5,7},{6,4},{7,5},{8,10},{9,11},{10,... | collective-permute-start | bytes 196616 | tf_op jit(solution)/shard_map/ppermute | solution.py:33
  71.6 1.8 %collective-permute-start.37 = (f32[64,256]{1,0:T(8,128)S(1)}, f32[64,256]{1,0:T(8,128)S(1)}, u32[]{:S(2)}, u32[]{:S(2)}) collective-permute-start(f32[64,256]{1,0:T(8,128)S(1)} %get-tuple-element.73.refs_5_), channel_id=1, source_target_pairs={{0,3},{1,2},{2,1},{3,0},{4,7},{5,6},{6,5},{7,4},{8,11},{9,10},{10,... | collective-permute-start | bytes 196616 | tf_op jit(solution)/shard_map/ppermute | solution.py:33
  73.5 0.6 constant_dynamic-update-slice_fusion.19
  74.2 2.6 %collective-permute-start.35 = (f32[64,256]{1,0:T(8,128)S(1)}, f32[64,256]{1,0:T(8,128)S(1)}, u32[]{:S(2)}, u32[]{:S(2)}) collective-permute-start(f32[64,256]{1,0:T(8,128)S(1)} %get-tuple-element.72), channel_id=1, source_target_pairs={{0,2},{1,3},{2,0},{3,1},{4,6},{5,7},{6,4},{7,5},{8,10},{9,11},{10,... | collective-permute-start | bytes 196616 | tf_op jit(solution)/shard_map/ppermute | solution.py:33
  76.8 1.8 %collective-permute-start.38 = (f32[64,256]{1,0:T(8,128)S(1)}, f32[64,256]{1,0:T(8,128)S(1)}, u32[]{:S(2)}, u32[]{:S(2)}) collective-permute-start(f32[64,256]{1,0:T(8,128)S(1)} %get-tuple-element.72), channel_id=1, source_target_pairs={{0,3},{1,2},{2,1},{3,0},{4,7},{5,6},{6,5},{7,4},{8,11},{9,10},{10,... | collective-permute-start | bytes 196616 | tf_op jit(solution)/shard_map/ppermute | solution.py:33
  78.7 0.6 constant_dynamic-update-slice_fusion.11
  79.3 2.6 %collective-permute-start.40 = (f32[64,256]{1,0:T(8,128)S(1)}, f32[64,256]{1,0:T(8,128)S(1)}, u32[]{:S(2)}, u32[]{:S(2)}) collective-permute-start(f32[64,256]{1,0:T(8,128)S(1)} %get-tuple-element.75), channel_id=1, source_target_pairs={{0,2},{1,3},{2,0},{3,1},{4,6},{5,7},{6,4},{7,5},{8,10},{9,11},{10,... | collective-permute-start | bytes 196616 | tf_op jit(solution)/shard_map/ppermute | solution.py:33
  82.0 1.8 %collective-permute-start.41 = (f32[64,256]{1,0:T(8,128)S(1)}, f32[64,256]{1,0:T(8,128)S(1)}, u32[]{:S(2)}, u32[]{:S(2)}) collective-permute-start(f32[64,256]{1,0:T(8,128)S(1)} %get-tuple-element.75), channel_id=1, source_target_pairs={{0,3},{1,2},{2,1},{3,0},{4,7},{5,6},{6,5},{7,4},{8,11},{9,10},{10,... | collective-permute-start | bytes 196616 | tf_op jit(solution)/shard_map/ppermute | solution.py:33
  84.5 4.2 %collective-permute-start.43 = (f32[64,256]{1,0:T(8,128)S(1)}, f32[64,256]{1,0:T(8,128)S(1)}, u32[]{:S(2)}, u32[]{:S(2)}) collective-permute-start(f32[64,256]{1,0:T(8,128)S(1)} %get-tuple-element.77.refs_6_), channel_id=1, source_target_pairs={{0,2},{1,3},{2,0},{3,1},{4,6},{5,7},{6,4},{7,5},{8,10},{9,11},{10,... | collective-permute-start | bytes 196616 | tf_op jit(solution)/shard_map/ppermute | solution.py:33
  88.7 1.4 %collective-permute-start.44 = (f32[64,256]{1,0:T(8,128)S(1)}, f32[64,256]{1,0:T(8,128)S(1)}, u32[]{:S(2)}, u32[]{:S(2)}) collective-permute-start(f32[64,256]{1,0:T(8,128)S(1)} %get-tuple-element.77.refs_6_), channel_id=1, source_target_pairs={{0,3},{1,2},{2,1},{3,0},{4,7},{5,6},{6,5},{7,4},{8,11},{9,10},{10,... | collective-permute-start | bytes 196616 | tf_op jit(solution)/shard_map/ppermute | solution.py:33
  90.9 3.1 %collective-permute-start.46 = (f32[64,256]{1,0:T(8,128)S(1)}, f32[64,256]{1,0:T(8,128)S(1)}, u32[]{:S(2)}, u32[]{:S(2)}) collective-permute-start(f32[64,256]{1,0:T(8,128)S(1)} %get-tuple-element.79.refs_7_), channel_id=1, source_target_pairs={{0,2},{1,3},{2,0},{3,1},{4,6},{5,7},{6,4},{7,5},{8,10},{9,11},{10,... | collective-permute-start | bytes 196616 | tf_op jit(solution)/shard_map/ppermute | solution.py:33
  93.9 1.4 %collective-permute-start.47 = (f32[64,256]{1,0:T(8,128)S(1)}, f32[64,256]{1,0:T(8,128)S(1)}, u32[]{:S(2)}, u32[]{:S(2)}) collective-permute-start(f32[64,256]{1,0:T(8,128)S(1)} %get-tuple-element.79.refs_7_), channel_id=1, source_target_pairs={{0,3},{1,2},{2,1},{3,0},{4,7},{5,6},{6,5},{7,4},{8,11},{9,10},{10,... | collective-permute-start | bytes 196616 | tf_op jit(solution)/shard_map/ppermute | solution.py:33
  95.4 1.0 collective-permute-done.46
  96.4 1.2 shard_map.117.refs_0_
  97.6 2.7 %collective-permute-done.45 = f32[64,256]{1,0:T(8,128)S(1)} collective-permute-done((f32[64,256]{1,0:T(8,128)S(1)}, f32[64,256]{1,0:T(8,128)S(1)}, u32[]{:S(2)}, u32[]{:S(2)}) %collective-permute-start.45) | collective-permute-done | bytes 65568 | tf_op jit(solution)/shard_map/ppermute | solution.py:33
  100.3 1.2 shard_map.118
  101.6 1.3 collective-permute-done.48.refs_1_
  103.0 2.5 %collective-permute-start.49 = (f32[2,16,512]{2,1,0:T(8,128)S(1)}, f32[2,16,512]{2,1,0:T(8,128)S(1)}, u32[]{:S(2)}, u32[]{:S(2)}) collective-permute-start(f32[2,16,512]{2,1,0:T(8,128)S(1)} %get-tuple-element.85), channel_id=1, source_target_pairs={{0,24},{4,28},{8,16},{12,20},{16,8},{20,12},{24,0},{28,4},{1,25},{... | collective-permute-start | bytes 196616 | tf_op jit(solution)/shard_map/ppermute | solution.py:81
  106.5 1.0 shard_map.119
  107.5 0.7 collective-permute-done.49.refs_1_
  108.2 1.5 %collective-permute-done.50.refs_2_ = f32[2,16,512]{2,1,0:T(8,128)S(1)} collective-permute-done((f32[2,16,512]{2,1,0:T(8,128)S(1)}, f32[2,16,512]{2,1,0:T(8,128)S(1)}, u32[]{:S(2)}, u32[]{:S(2)}) %collective-permute-start.50) | collective-permute-done | bytes 65568 | tf_op jit(solution)/shard_map/ppermute | solution.py:81
  110.7 1.9 %collective-permute-start.52 = (f32[16,1024]{1,0:T(8,128)S(1)}, f32[16,1024]{1,0:T(8,128)S(1)}, u32[]{:S(2)}, u32[]{:S(2)}) collective-permute-start(f32[16,1024]{1,0:T(8,128)S(1)} %get-tuple-element.89.refs_2_.refs_0_), channel_id=1, source_target_pairs={{0,3},{1,2},{2,1},{3,0},{4,7},{5,6},{6,5},{7,4},{8,11},{9,10},{10,... | collective-permute-start | bytes 196616 | tf_op jit(solution)/shard_map/ppermute | solution.py:33
  112.5 2.6 %collective-permute-start.54 = (f32[16,1024]{1,0:T(8,128)S(1)}, f32[16,1024]{1,0:T(8,128)S(1)}, u32[]{:S(2)}, u32[]{:S(2)}) collective-permute-start(f32[16,1024]{1,0:T(8,128)S(1)} %get-tuple-element.89.refs_2_.refs_0_), channel_id=1, source_target_pairs={{0,1},{1,0},{2,3},{3,2},{4,5},{5,4},{6,7},{7,6},{8,9},{9,8},{10,11... | collective-permute-start | bytes 196616 | tf_op jit(solution)/shard_map/ppermute | solution.py:33
  115.6 1.3 collective-permute-done.52.refs_1_
  116.9 1.6 %collective-permute-done.53.refs_2_ = f32[16,1024]{1,0:T(8,128)S(1)} collective-permute-done((f32[16,1024]{1,0:T(8,128)S(1)}, f32[16,1024]{1,0:T(8,128)S(1)}, u32[]{:S(2)}, u32[]{:S(2)}) %collective-permute-start.53) | collective-permute-done | bytes 65568 | tf_op jit(solution)/shard_map/ppermute | solution.py:33
  118.9 1.8 %collective-permute-start.55 = (f32[16,512]{1,0:T(8,128)S(1)}, f32[16,512]{1,0:T(8,128)S(1)}, u32[]{:S(2)}, u32[]{:S(2)}) collective-permute-start(f32[16,512]{1,0:T(8,128)S(1)} %get-tuple-element.97), channel_id=1, source_target_pairs={{0,3},{1,2},{2,1},{3,0},{4,7},{5,6},{6,5},{7,4},{8,11},{9,10},{10,... | collective-permute-start | bytes 98312 | tf_op jit(solution)/shard_map/ppermute | solution.py:33
  121.3 2.1 %collective-permute-start.57 = (f32[16,512]{1,0:T(8,128)S(1)}, f32[16,512]{1,0:T(8,128)S(1)}, u32[]{:S(2)}, u32[]{:S(2)}) collective-permute-start(f32[16,512]{1,0:T(8,128)S(1)} %get-tuple-element.99), channel_id=1, source_target_pairs={{0,1},{1,0},{2,3},{3,2},{4,5},{5,4},{6,7},{7,6},{8,9},{9,8},{10,11... | collective-permute-start | bytes 98312 | tf_op jit(solution)/shard_map/ppermute | solution.py:33
  123.4 1.4 %collective-permute-done.55.refs_2_ = f32[16,512]{1,0:T(8,128)S(1)} collective-permute-done((f32[16,512]{1,0:T(8,128)S(1)}, f32[16,512]{1,0:T(8,128)S(1)}, u32[]{:S(2)}, u32[]{:S(2)}) %collective-permute-start.55) | collective-permute-done | bytes 32800 | tf_op jit(solution)/shard_map/ppermute | solution.py:33
  124.8 0.9 collective-permute-done.56.refs_3_
  126.1 1.9 %collective-permute-start.58 = (f32[16,256]{1,0:T(8,128)S(1)}, f32[16,256]{1,0:T(8,128)S(1)}, u32[]{:S(2)}, u32[]{:S(2)}) collective-permute-start(f32[16,256]{1,0:T(8,128)S(1)} %shard_map.124.refs_0_), channel_id=1, source_target_pairs={{0,3},{1,2},{2,1},{3,0},{4,7},{5,6},{6,5},{7,4},{8,11},{9,10},{10,... | collective-permute-start | bytes 49160 | tf_op jit(solution)/shard_map/ppermute | solution.py:33
  128.0 1.1 collective-permute-start.59
  129.1 1.4 %collective-permute-start.60 = (f32[16,256]{1,0:T(8,128)S(1)}, f32[16,256]{1,0:T(8,128)S(1)}, u32[]{:S(2)}, u32[]{:S(2)}) collective-permute-start(f32[16,256]{1,0:T(8,128)S(1)} %shard_map.124.refs_0_), channel_id=1, source_target_pairs={{0,1},{1,0},{2,3},{3,2},{4,5},{5,4},{6,7},{7,6},{8,9},{9,8},{10,11... | collective-permute-start | bytes 49160 | tf_op jit(solution)/shard_map/ppermute | solution.py:33
  130.5 1.1 collective-permute-done.58.refs_1_
  131.7 1.2 collective-permute-done.59.refs_2_
  133.0 1.0 shard_map.125
  (162 shorter events, 12.4 us)
Async XLA Ops:
  1.7 26.2 %copy-start.3 = (f32[1,4,256,128]{3,2,1,0:T(8,128)S(1)}, f32[1,4,256,128]{3,2,1,0:T(8,128)}, u32[]{:S(2)}) copy-start(f32[1,4,256,128]{3,2,1,0:T(8,128)} %rhs_ref.3) | copy-start | bytes 1572868
  1.9 10.1 %collective-permute-start = (f32[64,256]{1,0:T(8,128)S(1)}, f32[64,256]{1,0:T(8,128)S(1)}, u32[]{:S(2)}, u32[]{:S(2)}) collective-permute-start(f32[64,256]{1,0:T(8,128)S(1)} %get-tuple-element.52.refs_0_), channel_id=1, source_target_pairs={{0,1},{1,0},{2,3},{3,2},{4,5},{5,4},{6,7},{7,6},{8,9},{9,8},{10,11... | collective-permute-start | bytes 196616 | tf_op jit(solution)/shard_map/ppermute | solution.py:33
  5.0 9.1 %collective-permute-start.1 = (f32[64,256]{1,0:T(8,128)S(1)}, f32[64,256]{1,0:T(8,128)S(1)}, u32[]{:S(2)}, u32[]{:S(2)}) collective-permute-start(f32[64,256]{1,0:T(8,128)S(1)} %get-tuple-element.52.refs_0_), channel_id=1, source_target_pairs={{0,2},{1,3},{2,0},{3,1},{4,6},{5,7},{6,4},{7,5},{8,10},{9,11},{10,... | collective-permute-start | bytes 196616 | tf_op jit(solution)/shard_map/ppermute | solution.py:33
  7.6 6.6 %collective-permute-start.2 = (f32[64,256]{1,0:T(8,128)S(1)}, f32[64,256]{1,0:T(8,128)S(1)}, u32[]{:S(2)}, u32[]{:S(2)}) collective-permute-start(f32[64,256]{1,0:T(8,128)S(1)} %get-tuple-element.52.refs_0_), channel_id=1, source_target_pairs={{0,3},{1,2},{2,1},{3,0},{4,7},{5,6},{6,5},{7,4},{8,11},{9,10},{10,... | collective-permute-start | bytes 196616 | tf_op jit(solution)/shard_map/ppermute | solution.py:33
  7.6 12.2 %collective-permute-start.3 = (f32[64,256]{1,0:T(8,128)S(1)}, f32[64,256]{1,0:T(8,128)S(1)}, u32[]{:S(2)}, u32[]{:S(2)}) collective-permute-start(f32[64,256]{1,0:T(8,128)S(1)} %get-tuple-element.53.refs_0_), channel_id=1, source_target_pairs={{0,1},{1,0},{2,3},{3,2},{4,5},{5,4},{6,7},{7,6},{8,9},{9,8},{10,11... | collective-permute-start | bytes 196616 | tf_op jit(solution)/shard_map/ppermute | solution.py:33
  8.5 12.7 %collective-permute-start.4 = (f32[64,256]{1,0:T(8,128)S(1)}, f32[64,256]{1,0:T(8,128)S(1)}, u32[]{:S(2)}, u32[]{:S(2)}) collective-permute-start(f32[64,256]{1,0:T(8,128)S(1)} %get-tuple-element.53.refs_0_), channel_id=1, source_target_pairs={{0,2},{1,3},{2,0},{3,1},{4,6},{5,7},{6,4},{7,5},{8,10},{9,11},{10,... | collective-permute-start | bytes 196616 | tf_op jit(solution)/shard_map/ppermute | solution.py:33
  12.0 9.2 %collective-permute-start.5 = (f32[64,256]{1,0:T(8,128)S(1)}, f32[64,256]{1,0:T(8,128)S(1)}, u32[]{:S(2)}, u32[]{:S(2)}) collective-permute-start(f32[64,256]{1,0:T(8,128)S(1)} %get-tuple-element.53.refs_0_), channel_id=1, source_target_pairs={{0,3},{1,2},{2,1},{3,0},{4,7},{5,6},{6,5},{7,4},{8,11},{9,10},{10,... | collective-permute-start | bytes 196616 | tf_op jit(solution)/shard_map/ppermute | solution.py:33
  14.6 13.2 %collective-permute-start.6 = (f32[64,256]{1,0:T(8,128)S(1)}, f32[64,256]{1,0:T(8,128)S(1)}, u32[]{:S(2)}, u32[]{:S(2)}) collective-permute-start(f32[64,256]{1,0:T(8,128)S(1)} %shard_map.114.refs_0_), channel_id=1, source_target_pairs={{0,1},{1,0},{2,3},{3,2},{4,5},{5,4},{6,7},{7,6},{8,9},{9,8},{10,11... | collective-permute-start | bytes 196616 | tf_op jit(solution)/shard_map/ppermute | solution.py:33
  17.7 10.2 %collective-permute-start.7 = (f32[64,256]{1,0:T(8,128)S(1)}, f32[64,256]{1,0:T(8,128)S(1)}, u32[]{:S(2)}, u32[]{:S(2)}) collective-permute-start(f32[64,256]{1,0:T(8,128)S(1)} %shard_map.114.refs_0_), channel_id=1, source_target_pairs={{0,2},{1,3},{2,0},{3,1},{4,6},{5,7},{6,4},{7,5},{8,10},{9,11},{10,... | collective-permute-start | bytes 196616 | tf_op jit(solution)/shard_map/ppermute | solution.py:33
  19.8 8.5 %collective-permute-start.8 = (f32[64,256]{1,0:T(8,128)S(1)}, f32[64,256]{1,0:T(8,128)S(1)}, u32[]{:S(2)}, u32[]{:S(2)}) collective-permute-start(f32[64,256]{1,0:T(8,128)S(1)} %shard_map.114.refs_0_), channel_id=1, source_target_pairs={{0,3},{1,2},{2,1},{3,0},{4,7},{5,6},{6,5},{7,4},{8,11},{9,10},{10,... | collective-permute-start | bytes 196616 | tf_op jit(solution)/shard_map/ppermute | solution.py:33
  21.7 11.8 %collective-permute-start.9 = (f32[64,256]{1,0:T(8,128)S(1)}, f32[64,256]{1,0:T(8,128)S(1)}, u32[]{:S(2)}, u32[]{:S(2)}) collective-permute-start(f32[64,256]{1,0:T(8,128)S(1)} %shard_map.115.refs_1_), channel_id=1, source_target_pairs={{0,2},{1,3},{2,0},{3,1},{4,6},{5,7},{6,4},{7,5},{8,10},{9,11},{10,... | collective-permute-start | bytes 196616 | tf_op jit(solution)/shard_map/ppermute | solution.py:33
  24.0 9.6 %collective-permute-start.13 = (f32[64,256]{1,0:T(8,128)S(1)}, f32[64,256]{1,0:T(8,128)S(1)}, u32[]{:S(2)}, u32[]{:S(2)}) collective-permute-start(f32[64,256]{1,0:T(8,128)S(1)} %shard_map.115.refs_1_), channel_id=1, source_target_pairs={{0,3},{1,2},{2,1},{3,0},{4,7},{5,6},{6,5},{7,4},{8,11},{9,10},{10,... | collective-permute-start | bytes 196616 | tf_op jit(solution)/shard_map/ppermute | solution.py:33
  27.9 5.6 %collective-permute-start.12 = (f32[64,256]{1,0:T(8,128)S(1)}, f32[64,256]{1,0:T(8,128)S(1)}, u32[]{:S(2)}, u32[]{:S(2)}) collective-permute-start(f32[64,256]{1,0:T(8,128)S(1)} %shard_map.115.refs_1_), channel_id=1, source_target_pairs={{0,1},{1,0},{2,3},{3,2},{4,5},{5,4},{6,7},{7,6},{8,9},{9,8},{10,11... | collective-permute-start | bytes 196616 | tf_op jit(solution)/shard_map/ppermute | solution.py:33
  29.0 9.6 %collective-permute-start.11 = (f32[64,256]{1,0:T(8,128)S(1)}, f32[64,256]{1,0:T(8,128)S(1)}, u32[]{:S(2)}, u32[]{:S(2)}) collective-permute-start(f32[64,256]{1,0:T(8,128)S(1)} %get-tuple-element.56), channel_id=1, source_target_pairs={{0,2},{1,3},{2,0},{3,1},{4,6},{5,7},{6,4},{7,5},{8,10},{9,11},{10,... | collective-permute-start | bytes 196616 | tf_op jit(solution)/shard_map/ppermute | solution.py:33
  32.9 6.8 %collective-permute-start.14 = (f32[64,256]{1,0:T(8,128)S(1)}, f32[64,256]{1,0:T(8,128)S(1)}, u32[]{:S(2)}, u32[]{:S(2)}) collective-permute-start(f32[64,256]{1,0:T(8,128)S(1)} %get-tuple-element.56), channel_id=1, source_target_pairs={{0,3},{1,2},{2,1},{3,0},{4,7},{5,6},{6,5},{7,4},{8,11},{9,10},{10,... | collective-permute-start | bytes 196616 | tf_op jit(solution)/shard_map/ppermute | solution.py:33
  33.4 5.2 %collective-permute-start.10 = (f32[64,256]{1,0:T(8,128)S(1)}, f32[64,256]{1,0:T(8,128)S(1)}, u32[]{:S(2)}, u32[]{:S(2)}) collective-permute-start(f32[64,256]{1,0:T(8,128)S(1)} %get-tuple-element.56), channel_id=1, source_target_pairs={{0,1},{1,0},{2,3},{3,2},{4,5},{5,4},{6,7},{7,6},{8,9},{9,8},{10,11... | collective-permute-start | bytes 196616 | tf_op jit(solution)/shard_map/ppermute | solution.py:33
  34.2 9.7 %collective-permute-start.16 = (f32[64,256]{1,0:T(8,128)S(1)}, f32[64,256]{1,0:T(8,128)S(1)}, u32[]{:S(2)}, u32[]{:S(2)}) collective-permute-start(f32[64,256]{1,0:T(8,128)S(1)} %get-tuple-element.59), channel_id=1, source_target_pairs={{0,2},{1,3},{2,0},{3,1},{4,6},{5,7},{6,4},{7,5},{8,10},{9,11},{10,... | collective-permute-start | bytes 196616 | tf_op jit(solution)/shard_map/ppermute | solution.py:33
  38.0 6.3 %collective-permute-start.17 = (f32[64,256]{1,0:T(8,128)S(1)}, f32[64,256]{1,0:T(8,128)S(1)}, u32[]{:S(2)}, u32[]{:S(2)}) collective-permute-start(f32[64,256]{1,0:T(8,128)S(1)} %get-tuple-element.59), channel_id=1, source_target_pairs={{0,3},{1,2},{2,1},{3,0},{4,7},{5,6},{6,5},{7,4},{8,11},{9,10},{10,... | collective-permute-start | bytes 196616 | tf_op jit(solution)/shard_map/ppermute | solution.py:33
  38.6 5.7 %collective-permute-start.15 = (f32[64,256]{1,0:T(8,128)S(1)}, f32[64,256]{1,0:T(8,128)S(1)}, u32[]{:S(2)}, u32[]{:S(2)}) collective-permute-start(f32[64,256]{1,0:T(8,128)S(1)} %get-tuple-element.59), channel_id=1, source_target_pairs={{0,1},{1,0},{2,3},{3,2},{4,5},{5,4},{6,7},{7,6},{8,9},{9,8},{10,11... | collective-permute-start | bytes 196616 | tf_op jit(solution)/shard_map/ppermute | solution.py:33
  40.4 10.5 %collective-permute-start.19 = (f32[64,256]{1,0:T(8,128)S(1)}, f32[64,256]{1,0:T(8,128)S(1)}, u32[]{:S(2)}, u32[]{:S(2)}) collective-permute-start(f32[64,256]{1,0:T(8,128)S(1)} %get-tuple-element.61.refs_2_), channel_id=1, source_target_pairs={{0,2},{1,3},{2,0},{3,1},{4,6},{5,7},{6,4},{7,5},{8,10},{9,11},{10,... | collective-permute-start | bytes 196616 | tf_op jit(solution)/shard_map/ppermute | solution.py:33
  43.2 7.7 %collective-permute-start.20 = (f32[64,256]{1,0:T(8,128)S(1)}, f32[64,256]{1,0:T(8,128)S(1)}, u32[]{:S(2)}, u32[]{:S(2)}) collective-permute-start(f32[64,256]{1,0:T(8,128)S(1)} %get-tuple-element.61.refs_2_), channel_id=1, source_target_pairs={{0,3},{1,2},{2,1},{3,0},{4,7},{5,6},{6,5},{7,4},{8,11},{9,10},{10,... | collective-permute-start | bytes 196616 | tf_op jit(solution)/shard_map/ppermute | solution.py:33
  43.9 7.0 %collective-permute-start.18 = (f32[64,256]{1,0:T(8,128)S(1)}, f32[64,256]{1,0:T(8,128)S(1)}, u32[]{:S(2)}, u32[]{:S(2)}) collective-permute-start(f32[64,256]{1,0:T(8,128)S(1)} %get-tuple-element.61.refs_2_), channel_id=1, source_target_pairs={{0,1},{1,0},{2,3},{3,2},{4,5},{5,4},{6,7},{7,6},{8,9},{9,8},{10,11... | collective-permute-start | bytes 196616 | tf_op jit(solution)/shard_map/ppermute | solution.py:33
  45.0 11.0 %collective-permute-start.21 = (f32[64,256]{1,0:T(8,128)S(1)}, f32[64,256]{1,0:T(8,128)S(1)}, u32[]{:S(2)}, u32[]{:S(2)}) collective-permute-start(f32[64,256]{1,0:T(8,128)S(1)} %get-tuple-element.65.refs_3_), channel_id=1, source_target_pairs={{0,2},{1,3},{2,0},{3,1},{4,6},{5,7},{6,4},{7,5},{8,10},{9,11},{10,... | collective-permute-start | bytes 196616 | tf_op jit(solution)/shard_map/ppermute | solution.py:33
  49.0 7.1 %collective-permute-start.25 = (f32[64,256]{1,0:T(8,128)S(1)}, f32[64,256]{1,0:T(8,128)S(1)}, u32[]{:S(2)}, u32[]{:S(2)}) collective-permute-start(f32[64,256]{1,0:T(8,128)S(1)} %get-tuple-element.65.refs_3_), channel_id=1, source_target_pairs={{0,3},{1,2},{2,1},{3,0},{4,7},{5,6},{6,5},{7,4},{8,11},{9,10},{10,... | collective-permute-start | bytes 196616 | tf_op jit(solution)/shard_map/ppermute | solution.py:33
  50.9 5.2 %collective-permute-start.24 = (f32[64,256]{1,0:T(8,128)S(1)}, f32[64,256]{1,0:T(8,128)S(1)}, u32[]{:S(2)}, u32[]{:S(2)}) collective-permute-start(f32[64,256]{1,0:T(8,128)S(1)} %get-tuple-element.65.refs_3_), channel_id=1, source_target_pairs={{0,1},{1,0},{2,3},{3,2},{4,5},{5,4},{6,7},{7,6},{8,9},{9,8},{10,11... | collective-permute-start | bytes 196616 | tf_op jit(solution)/shard_map/ppermute | solution.py:33
  51.6 9.6 %collective-permute-start.23 = (f32[64,256]{1,0:T(8,128)S(1)}, f32[64,256]{1,0:T(8,128)S(1)}, u32[]{:S(2)}, u32[]{:S(2)}) collective-permute-start(f32[64,256]{1,0:T(8,128)S(1)} %get-tuple-element.64), channel_id=1, source_target_pairs={{0,2},{1,3},{2,0},{3,1},{4,6},{5,7},{6,4},{7,5},{8,10},{9,11},{10,... | collective-permute-start | bytes 196616 | tf_op jit(solution)/shard_map/ppermute | solution.py:33
  54.2 7.1 %collective-permute-start.26 = (f32[64,256]{1,0:T(8,128)S(1)}, f32[64,256]{1,0:T(8,128)S(1)}, u32[]{:S(2)}, u32[]{:S(2)}) collective-permute-start(f32[64,256]{1,0:T(8,128)S(1)} %get-tuple-element.64), channel_id=1, source_target_pairs={{0,3},{1,2},{2,1},{3,0},{4,7},{5,6},{6,5},{7,4},{8,11},{9,10},{10,... | collective-permute-start | bytes 196616 | tf_op jit(solution)/shard_map/ppermute | solution.py:33
  56.1 5.2 %collective-permute-start.22 = (f32[64,256]{1,0:T(8,128)S(1)}, f32[64,256]{1,0:T(8,128)S(1)}, u32[]{:S(2)}, u32[]{:S(2)}) collective-permute-start(f32[64,256]{1,0:T(8,128)S(1)} %get-tuple-element.64), channel_id=1, source_target_pairs={{0,1},{1,0},{2,3},{3,2},{4,5},{5,4},{6,7},{7,6},{8,9},{9,8},{10,11... | collective-permute-start | bytes 196616 | tf_op jit(solution)/shard_map/ppermute | solution.py:33
  56.8 9.6 %collective-permute-start.28 = (f32[64,256]{1,0:T(8,128)S(1)}, f32[64,256]{1,0:T(8,128)S(1)}, u32[]{:S(2)}, u32[]{:S(2)}) collective-permute-start(f32[64,256]{1,0:T(8,128)S(1)} %get-tuple-element.67), channel_id=1, source_target_pairs={{0,2},{1,3},{2,0},{3,1},{4,6},{5,7},{6,4},{7,5},{8,10},{9,11},{10,... | collective-permute-start | bytes 196616 | tf_op jit(solution)/shard_map/ppermute | solution.py:33
  60.4 6.5 %collective-permute-start.29 = (f32[64,256]{1,0:T(8,128)S(1)}, f32[64,256]{1,0:T(8,128)S(1)}, u32[]{:S(2)}, u32[]{:S(2)}) collective-permute-start(f32[64,256]{1,0:T(8,128)S(1)} %get-tuple-element.67), channel_id=1, source_target_pairs={{0,3},{1,2},{2,1},{3,0},{4,7},{5,6},{6,5},{7,4},{8,11},{9,10},{10,... | collective-permute-start | bytes 196616 | tf_op jit(solution)/shard_map/ppermute | solution.py:33
  61.3 5.7 %collective-permute-start.27 = (f32[64,256]{1,0:T(8,128)S(1)}, f32[64,256]{1,0:T(8,128)S(1)}, u32[]{:S(2)}, u32[]{:S(2)}) collective-permute-start(f32[64,256]{1,0:T(8,128)S(1)} %get-tuple-element.67), channel_id=1, source_target_pairs={{0,1},{1,0},{2,3},{3,2},{4,5},{5,4},{6,7},{7,6},{8,9},{9,8},{10,11... | collective-permute-start | bytes 196616 | tf_op jit(solution)/shard_map/ppermute | solution.py:33
  62.0 11.4 %collective-permute-start.31 = (f32[64,256]{1,0:T(8,128)S(1)}, f32[64,256]{1,0:T(8,128)S(1)}, u32[]{:S(2)}, u32[]{:S(2)}) collective-permute-start(f32[64,256]{1,0:T(8,128)S(1)} %get-tuple-element.69.refs_4_), channel_id=1, source_target_pairs={{0,2},{1,3},{2,0},{3,1},{4,6},{5,7},{6,4},{7,5},{8,10},{9,11},{10,... | collective-permute-start | bytes 196616 | tf_op jit(solution)/shard_map/ppermute | solution.py:33
  65.6 7.9 %collective-permute-start.32 = (f32[64,256]{1,0:T(8,128)S(1)}, f32[64,256]{1,0:T(8,128)S(1)}, u32[]{:S(2)}, u32[]{:S(2)}) collective-permute-start(f32[64,256]{1,0:T(8,128)S(1)} %get-tuple-element.69.refs_4_), channel_id=1, source_target_pairs={{0,3},{1,2},{2,1},{3,0},{4,7},{5,6},{6,5},{7,4},{8,11},{9,10},{10,... | collective-permute-start | bytes 196616 | tf_op jit(solution)/shard_map/ppermute | solution.py:33
  66.4 7.0 %collective-permute-start.30 = (f32[64,256]{1,0:T(8,128)S(1)}, f32[64,256]{1,0:T(8,128)S(1)}, u32[]{:S(2)}, u32[]{:S(2)}) collective-permute-start(f32[64,256]{1,0:T(8,128)S(1)} %get-tuple-element.69.refs_4_), channel_id=1, source_target_pairs={{0,1},{1,0},{2,3},{3,2},{4,5},{5,4},{6,7},{7,6},{8,9},{9,8},{10,11... | collective-permute-start | bytes 196616 | tf_op jit(solution)/shard_map/ppermute | solution.py:33
  67.6 11.0 %collective-permute-start.33 = (f32[64,256]{1,0:T(8,128)S(1)}, f32[64,256]{1,0:T(8,128)S(1)}, u32[]{:S(2)}, u32[]{:S(2)}) collective-permute-start(f32[64,256]{1,0:T(8,128)S(1)} %get-tuple-element.73.refs_5_), channel_id=1, source_target_pairs={{0,2},{1,3},{2,0},{3,1},{4,6},{5,7},{6,4},{7,5},{8,10},{9,11},{10,... | collective-permute-start | bytes 196616 | tf_op jit(solution)/shard_map/ppermute | solution.py:33
  71.6 7.1 %collective-permute-start.37 = (f32[64,256]{1,0:T(8,128)S(1)}, f32[64,256]{1,0:T(8,128)S(1)}, u32[]{:S(2)}, u32[]{:S(2)}) collective-permute-start(f32[64,256]{1,0:T(8,128)S(1)} %get-tuple-element.73.refs_5_), channel_id=1, source_target_pairs={{0,3},{1,2},{2,1},{3,0},{4,7},{5,6},{6,5},{7,4},{8,11},{9,10},{10,... | collective-permute-start | bytes 196616 | tf_op jit(solution)/shard_map/ppermute | solution.py:33
  73.4 5.2 %collective-permute-start.36 = (f32[64,256]{1,0:T(8,128)S(1)}, f32[64,256]{1,0:T(8,128)S(1)}, u32[]{:S(2)}, u32[]{:S(2)}) collective-permute-start(f32[64,256]{1,0:T(8,128)S(1)} %get-tuple-element.73.refs_5_), channel_id=1, source_target_pairs={{0,1},{1,0},{2,3},{3,2},{4,5},{5,4},{6,7},{7,6},{8,9},{9,8},{10,11... | collective-permute-start | bytes 196616 | tf_op jit(solution)/shard_map/ppermute | solution.py:33
  74.2 9.6 %collective-permute-start.35 = (f32[64,256]{1,0:T(8,128)S(1)}, f32[64,256]{1,0:T(8,128)S(1)}, u32[]{:S(2)}, u32[]{:S(2)}) collective-permute-start(f32[64,256]{1,0:T(8,128)S(1)} %get-tuple-element.72), channel_id=1, source_target_pairs={{0,2},{1,3},{2,0},{3,1},{4,6},{5,7},{6,4},{7,5},{8,10},{9,11},{10,... | collective-permute-start | bytes 196616 | tf_op jit(solution)/shard_map/ppermute | solution.py:33
  76.8 7.1 %collective-permute-start.38 = (f32[64,256]{1,0:T(8,128)S(1)}, f32[64,256]{1,0:T(8,128)S(1)}, u32[]{:S(2)}, u32[]{:S(2)}) collective-permute-start(f32[64,256]{1,0:T(8,128)S(1)} %get-tuple-element.72), channel_id=1, source_target_pairs={{0,3},{1,2},{2,1},{3,0},{4,7},{5,6},{6,5},{7,4},{8,11},{9,10},{10,... | collective-permute-start | bytes 196616 | tf_op jit(solution)/shard_map/ppermute | solution.py:33
  78.6 5.2 %collective-permute-start.34 = (f32[64,256]{1,0:T(8,128)S(1)}, f32[64,256]{1,0:T(8,128)S(1)}, u32[]{:S(2)}, u32[]{:S(2)}) collective-permute-start(f32[64,256]{1,0:T(8,128)S(1)} %get-tuple-element.72), channel_id=1, source_target_pairs={{0,1},{1,0},{2,3},{3,2},{4,5},{5,4},{6,7},{7,6},{8,9},{9,8},{10,11... | collective-permute-start | bytes 196616 | tf_op jit(solution)/shard_map/ppermute | solution.py:33
  79.3 10.8 %collective-permute-start.40 = (f32[64,256]{1,0:T(8,128)S(1)}, f32[64,256]{1,0:T(8,128)S(1)}, u32[]{:S(2)}, u32[]{:S(2)}) collective-permute-start(f32[64,256]{1,0:T(8,128)S(1)} %get-tuple-element.75), channel_id=1, source_target_pairs={{0,2},{1,3},{2,0},{3,1},{4,6},{5,7},{6,4},{7,5},{8,10},{9,11},{10,... | collective-permute-start | bytes 196616 | tf_op jit(solution)/shard_map/ppermute | solution.py:33
  82.0 8.2 %collective-permute-start.41 = (f32[64,256]{1,0:T(8,128)S(1)}, f32[64,256]{1,0:T(8,128)S(1)}, u32[]{:S(2)}, u32[]{:S(2)}) collective-permute-start(f32[64,256]{1,0:T(8,128)S(1)} %get-tuple-element.75), channel_id=1, source_target_pairs={{0,3},{1,2},{2,1},{3,0},{4,7},{5,6},{6,5},{7,4},{8,11},{9,10},{10,... | collective-permute-start | bytes 196616 | tf_op jit(solution)/shard_map/ppermute | solution.py:33
  83.8 6.3 %collective-permute-start.39 = (f32[64,256]{1,0:T(8,128)S(1)}, f32[64,256]{1,0:T(8,128)S(1)}, u32[]{:S(2)}, u32[]{:S(2)}) collective-permute-start(f32[64,256]{1,0:T(8,128)S(1)} %get-tuple-element.75), channel_id=1, source_target_pairs={{0,1},{1,0},{2,3},{3,2},{4,5},{5,4},{6,7},{7,6},{8,9},{9,8},{10,11... | collective-permute-start | bytes 196616 | tf_op jit(solution)/shard_map/ppermute | solution.py:33
  84.5 10.8 %collective-permute-start.43 = (f32[64,256]{1,0:T(8,128)S(1)}, f32[64,256]{1,0:T(8,128)S(1)}, u32[]{:S(2)}, u32[]{:S(2)}) collective-permute-start(f32[64,256]{1,0:T(8,128)S(1)} %get-tuple-element.77.refs_6_), channel_id=1, source_target_pairs={{0,2},{1,3},{2,0},{3,1},{4,6},{5,7},{6,4},{7,5},{8,10},{9,11},{10,... | collective-permute-start | bytes 196616 | tf_op jit(solution)/shard_map/ppermute | solution.py:33
  88.7 6.6 %collective-permute-start.44 = (f32[64,256]{1,0:T(8,128)S(1)}, f32[64,256]{1,0:T(8,128)S(1)}, u32[]{:S(2)}, u32[]{:S(2)}) collective-permute-start(f32[64,256]{1,0:T(8,128)S(1)} %get-tuple-element.77.refs_6_), channel_id=1, source_target_pairs={{0,3},{1,2},{2,1},{3,0},{4,7},{5,6},{6,5},{7,4},{8,11},{9,10},{10,... | collective-permute-start | bytes 196616 | tf_op jit(solution)/shard_map/ppermute | solution.py:33
  90.1 5.2 %collective-permute-start.42 = (f32[64,256]{1,0:T(8,128)S(1)}, f32[64,256]{1,0:T(8,128)S(1)}, u32[]{:S(2)}, u32[]{:S(2)}) collective-permute-start(f32[64,256]{1,0:T(8,128)S(1)} %get-tuple-element.77.refs_6_), channel_id=1, source_target_pairs={{0,1},{1,0},{2,3},{3,2},{4,5},{5,4},{6,7},{7,6},{8,9},{9,8},{10,11... | collective-permute-start | bytes 196616 | tf_op jit(solution)/shard_map/ppermute | solution.py:33
  90.9 5.5 %collective-permute-start.46 = (f32[64,256]{1,0:T(8,128)S(1)}, f32[64,256]{1,0:T(8,128)S(1)}, u32[]{:S(2)}, u32[]{:S(2)}) collective-permute-start(f32[64,256]{1,0:T(8,128)S(1)} %get-tuple-element.79.refs_7_), channel_id=1, source_target_pairs={{0,2},{1,3},{2,0},{3,1},{4,6},{5,7},{6,4},{7,5},{8,10},{9,11},{10,... | collective-permute-start | bytes 196616 | tf_op jit(solution)/shard_map/ppermute | solution.py:33
  93.9 6.4 %collective-permute-start.47 = (f32[64,256]{1,0:T(8,128)S(1)}, f32[64,256]{1,0:T(8,128)S(1)}, u32[]{:S(2)}, u32[]{:S(2)}) collective-permute-start(f32[64,256]{1,0:T(8,128)S(1)} %get-tuple-element.79.refs_7_), channel_id=1, source_target_pairs={{0,3},{1,2},{2,1},{3,0},{4,7},{5,6},{6,5},{7,4},{8,11},{9,10},{10,... | collective-permute-start | bytes 196616 | tf_op jit(solution)/shard_map/ppermute | solution.py:33
  95.3 5.0 %collective-permute-start.45 = (f32[64,256]{1,0:T(8,128)S(1)}, f32[64,256]{1,0:T(8,128)S(1)}, u32[]{:S(2)}, u32[]{:S(2)}) collective-permute-start(f32[64,256]{1,0:T(8,128)S(1)} %get-tuple-element.79.refs_7_), channel_id=1, source_target_pairs={{0,1},{1,0},{2,3},{3,2},{4,5},{5,4},{6,7},{7,6},{8,9},{9,8},{10,11... | collective-permute-start | bytes 196616 | tf_op jit(solution)/shard_map/ppermute | solution.py:33
  96.3 18.8 %copy-start.1 = (f32[2,256,1024]{2,1,0:T(8,128)S(1)}, f32[2,256,1024]{2,1,0:T(8,128)}, u32[]{:S(2)}) copy-start(f32[2,256,1024]{2,1,0:T(8,128)} %refs_0_.1) | copy-start | bytes 6291460
  96.4 18.8 %copy-start.4 = (f32[1,256,1024]{2,1,0:T(8,128)S(1)}, f32[1,256,1024]{2,1,0:T(8,128)}, u32[]{:S(2)}) copy-start(f32[1,256,1024]{2,1,0:T(8,128)} %refs_1_.1) | copy-start | bytes 3145732
  101.5 1.4 %collective-permute-start.48 = (f32[4,16,512]{2,1,0:T(8,128)S(1)}, f32[4,16,512]{2,1,0:T(8,128)S(1)}, u32[]{:S(2)}, u32[]{:S(2)}) collective-permute-start(f32[4,16,512]{2,1,0:T(8,128)S(1)} %get-tuple-element.83), channel_id=1, source_target_pairs={{0,4},{4,0},{8,12},{12,8},{16,20},{20,16},{24,28},{28,24},{1,5},{5... | collective-permute-start | bytes 393224 | tf_op jit(solution)/shard_map/ppermute | solution.py:281
  103.0 5.3 %collective-permute-start.49 = (f32[2,16,512]{2,1,0:T(8,128)S(1)}, f32[2,16,512]{2,1,0:T(8,128)S(1)}, u32[]{:S(2)}, u32[]{:S(2)}) collective-permute-start(f32[2,16,512]{2,1,0:T(8,128)S(1)} %get-tuple-element.85), channel_id=1, source_target_pairs={{0,24},{4,28},{8,16},{12,20},{16,8},{20,12},{24,0},{28,4},{1,25},{... | collective-permute-start | bytes 196616 | tf_op jit(solution)/shard_map/ppermute | solution.py:81
  105.5 4.3 %collective-permute-start.50 = (f32[2,16,512]{2,1,0:T(8,128)S(1)}, f32[2,16,512]{2,1,0:T(8,128)S(1)}, u32[]{:S(2)}, u32[]{:S(2)}) collective-permute-start(f32[2,16,512]{2,1,0:T(8,128)S(1)} %get-tuple-element.86), channel_id=1, source_target_pairs={{0,16},{4,20},{8,24},{12,28},{16,0},{20,4},{24,8},{28,12},{1,17},{... | collective-permute-start | bytes 196616 | tf_op jit(solution)/shard_map/ppermute | solution.py:81
  106.0 4.3 %collective-permute-start.51 = (f32[2,16,512]{2,1,0:T(8,128)S(1)}, f32[2,16,512]{2,1,0:T(8,128)S(1)}, u32[]{:S(2)}, u32[]{:S(2)}) collective-permute-start(f32[2,16,512]{2,1,0:T(8,128)S(1)} %get-tuple-element.87), channel_id=1, source_target_pairs={{0,8},{4,12},{8,0},{12,4},{16,24},{20,28},{24,16},{28,20},{1,9},{5... | collective-permute-start | bytes 196616 | tf_op jit(solution)/shard_map/ppermute | solution.py:81
  110.7 6.3 %collective-permute-start.52 = (f32[16,1024]{1,0:T(8,128)S(1)}, f32[16,1024]{1,0:T(8,128)S(1)}, u32[]{:S(2)}, u32[]{:S(2)}) collective-permute-start(f32[16,1024]{1,0:T(8,128)S(1)} %get-tuple-element.89.refs_2_.refs_0_), channel_id=1, source_target_pairs={{0,3},{1,2},{2,1},{3,0},{4,7},{5,6},{6,5},{7,4},{8,11},{9,10},{10,... | collective-permute-start | bytes 196616 | tf_op jit(solution)/shard_map/ppermute | solution.py:33
  112.5 6.0 %collective-permute-start.53 = (f32[16,1024]{1,0:T(8,128)S(1)}, f32[16,1024]{1,0:T(8,128)S(1)}, u32[]{:S(2)}, u32[]{:S(2)}) collective-permute-start(f32[16,1024]{1,0:T(8,128)S(1)} %get-tuple-element.89.refs_2_.refs_0_), channel_id=1, source_target_pairs={{0,2},{1,3},{2,0},{3,1},{4,6},{5,7},{6,4},{7,5},{8,10},{9,11},{10,... | collective-permute-start | bytes 196616 | tf_op jit(solution)/shard_map/ppermute | solution.py:33
  112.5 6.0 %collective-permute-start.54 = (f32[16,1024]{1,0:T(8,128)S(1)}, f32[16,1024]{1,0:T(8,128)S(1)}, u32[]{:S(2)}, u32[]{:S(2)}) collective-permute-start(f32[16,1024]{1,0:T(8,128)S(1)} %get-tuple-element.89.refs_2_.refs_0_), channel_id=1, source_target_pairs={{0,1},{1,0},{2,3},{3,2},{4,5},{5,4},{6,7},{7,6},{8,9},{9,8},{10,11... | collective-permute-start | bytes 196616 | tf_op jit(solution)/shard_map/ppermute | solution.py:33
  118.9 5.8 %collective-permute-start.55 = (f32[16,512]{1,0:T(8,128)S(1)}, f32[16,512]{1,0:T(8,128)S(1)}, u32[]{:S(2)}, u32[]{:S(2)}) collective-permute-start(f32[16,512]{1,0:T(8,128)S(1)} %get-tuple-element.97), channel_id=1, source_target_pairs={{0,3},{1,2},{2,1},{3,0},{4,7},{5,6},{6,5},{7,4},{8,11},{9,10},{10,... | collective-permute-start | bytes 98312 | tf_op jit(solution)/shard_map/ppermute | solution.py:33
  120.8 4.9 %collective-permute-start.56 = (f32[16,512]{1,0:T(8,128)S(1)}, f32[16,512]{1,0:T(8,128)S(1)}, u32[]{:S(2)}, u32[]{:S(2)}) collective-permute-start(f32[16,512]{1,0:T(8,128)S(1)} %get-tuple-element.98), channel_id=1, source_target_pairs={{0,2},{1,3},{2,0},{3,1},{4,6},{5,7},{6,4},{7,5},{8,10},{9,11},{10,... | collective-permute-start | bytes 98312 | tf_op jit(solution)/shard_map/ppermute | solution.py:33
  121.3 4.5 %collective-permute-start.57 = (f32[16,512]{1,0:T(8,128)S(1)}, f32[16,512]{1,0:T(8,128)S(1)}, u32[]{:S(2)}, u32[]{:S(2)}) collective-permute-start(f32[16,512]{1,0:T(8,128)S(1)} %get-tuple-element.99), channel_id=1, source_target_pairs={{0,1},{1,0},{2,3},{3,2},{4,5},{5,4},{6,7},{7,6},{8,9},{9,8},{10,11... | collective-permute-start | bytes 98312 | tf_op jit(solution)/shard_map/ppermute | solution.py:33
  126.1 5.6 %collective-permute-start.58 = (f32[16,256]{1,0:T(8,128)S(1)}, f32[16,256]{1,0:T(8,128)S(1)}, u32[]{:S(2)}, u32[]{:S(2)}) collective-permute-start(f32[16,256]{1,0:T(8,128)S(1)} %shard_map.124.refs_0_), channel_id=1, source_target_pairs={{0,3},{1,2},{2,1},{3,0},{4,7},{5,6},{6,5},{7,4},{8,11},{9,10},{10,... | collective-permute-start | bytes 49160 | tf_op jit(solution)/shard_map/ppermute | solution.py:33
  128.0 4.8 %collective-permute-start.59 = (f32[16,256]{1,0:T(8,128)S(1)}, f32[16,256]{1,0:T(8,128)S(1)}, u32[]{:S(2)}, u32[]{:S(2)}) collective-permute-start(f32[16,256]{1,0:T(8,128)S(1)} %shard_map.124.refs_0_), channel_id=1, source_target_pairs={{0,2},{1,3},{2,0},{3,1},{4,6},{5,7},{6,4},{7,5},{8,10},{9,11},{10,... | collective-permute-start | bytes 49160 | tf_op jit(solution)/shard_map/ppermute | solution.py:33
  129.1 3.9 %collective-permute-start.60 = (f32[16,256]{1,0:T(8,128)S(1)}, f32[16,256]{1,0:T(8,128)S(1)}, u32[]{:S(2)}, u32[]{:S(2)}) collective-permute-start(f32[16,256]{1,0:T(8,128)S(1)} %shard_map.124.refs_0_), channel_id=1, source_target_pairs={{0,1},{1,0},{2,3},{3,2},{4,5},{5,4},{6,7},{7,6},{8,9},{9,8},{10,11... | collective-permute-start | bytes 49160 | tf_op jit(solution)/shard_map/ppermute | solution.py:33
  (7 other events, 95.4 us)
